TPU v7x, 32 devices: a whole 2x2x4 slice. The times are simulated.
32 devices in a mesh: grp: 2 (over y), row: 8 (over z, x), col: 2 (over core).
Axes of the slice: x: 2, y: 2, z: 4, core: 2. Of those that a mesh axis runs over, the one named last changes fastest.
Arguments:
- activations: bfloat16 [8192, 8192], P(('grp', 'row'), 'col'), parts along dimension 0, may hold values from -2 to 2, as said below
- start_sketch: bfloat16 [8192, 128], P(('grp', 'row')), parts along dimension 0, may hold values from -4 to 4, as said below
Outputs:
- basis: float32 [8192, 128], P(('grp', 'row')), parts along dimension 0
- projection: float32 [256, 8192], P(('grp', 'row'), 'col'), parts along dimension 0
There are 2 independent parts, one for each index of `grp`. A program takes and returns all parts, laid end to end along the dimension named above; each array names one. Nothing has to cross between parts.
Inputs may be any that keep to these rules, and one draw needn't show every extreme that they name: Real-valued activations with row and column scales that vary. `start_sketch`: Real-valued entries of order one.
All inputs are finite; a program needn't handle non-finite values.
Results may differ from a plain program's by a relative error of at most 0.0027.
Values may be sent and summed in bfloat16 or wider, within the bound.
No kernel may reach another device: no remote copies, remote signals or barrier semaphores. Data moves between devices by JAX's collectives and lax.ppermute only.
A program may use at most 64 MiB of HBM per device.

v0:
```python
import math

import jax
import jax.numpy as jnp
from jax import lax
from jax.sharding import PartitionSpec as P


def per_device(activations, start_sketch):
    rows_here = activations.shape[0]
    cols_here = activations.shape[1]
    width = start_sketch.shape[1]
    total_rows = rows_here * lax.axis_size("row")
    total_cols = cols_here * lax.axis_size("col")
    root_rows = math.sqrt(total_rows)
    block = activations
    shares = lax.psum_scatter(
        lax.dot_general(
            block, start_sketch, (((0,), (0,)), ((), ())), preferred_element_type=jnp.float32
        ),
        "row",
        scatter_dimension=0,
        tiled=True,
    )
    sketch_cols = (shares / root_rows).astype(jnp.bfloat16)
    block = activations
    partial_sketch = jnp.dot(
        block,
        lax.all_gather(sketch_cols, "row", axis=0, tiled=True),
        preferred_element_type=jnp.float32,
    )
    sketch = lax.psum(partial_sketch, "col") / total_cols
    local_gram = lax.dot_general(
        sketch, sketch, (((0,), (0,)), ((), ())), precision=lax.Precision.HIGHEST
    )
    gram = lax.psum(local_gram, "row")
    factor = jnp.linalg.cholesky(gram)
    solved = jax.scipy.linalg.solve_triangular(factor, sketch.T, lower=True)
    basis = solved.T * root_rows
    basis_low = basis.astype(jnp.bfloat16)
    share_rows = width // lax.axis_size("row")
    local_proj = lax.dot_general(
        basis_low, activations, (((0,), (0,)), ((), ())), preferred_element_type=jnp.float32
    )
    summed = lax.psum(local_proj, "row")
    projection = (
        lax.dynamic_slice_in_dim(summed, lax.axis_index("row") * share_rows, share_rows, 0)
        / total_rows
    )
    return (basis, projection)


def solution(mesh):
    return jax.shard_map(
        per_device,
        mesh=mesh,
        in_specs=(P(("grp", "row"), "col"), P(("grp", "row"), None)),
        out_specs=(P(("grp", "row"), None), P(("grp", "row"), "col")),
        check_vma=False,
    )
```

profile of v0, /device:TPU:0, one launch (start us, length us, event | category | flops | bytes accessed | tf_op | source)
XLA Modules:
  0.0 362.4 jit_solution(12760193661350857184)
XLA Ops:
  7.2 0.0 copy-start
  7.2 0.0 reduce-scatter.2.cloned.1.call-start
  7.2 0.8 copy-done
  8.1 4.8 %fusion.12 = f32[4096,128]{1,0:T(8,128)} fusion(bf16[512,4096]{1,0:T(8,128)(2,1)} %param.2, bf16[512,128]{1,0:T(8,128)(2,1)S(1)} %copy-done), kind=kOutput, calls=%fused_computation.22 | convolution fusion | flops 536870912 | bytes 6422528 | tf_op jit(solution)/shard_map/dot_general | solution.py:18
  12.9 0.0 reduce-scatter.2.cloned.1.call-update
  12.9 0.0 all-gather.2.cloned.1.call-start
  13.0 70.9 %reduce-scatter.2.cloned.1.call-done = f32[512,128]{1,0:T(8,128)} async-done(((f32[4096,128]{1,0:T(8,128)}), f32[512,128]{1,0:T(8,128)}) %reduce-scatter.2.cloned.1.call-update) | async-done | bytes 262160 | tf_op jit(solution)/shard_map/reduce_scatter | solution.py:17
  83.9 1.6 multiply_convert_fusion
  85.5 0.0 all-gather.2.cloned.1.call-update
  85.6 0.0 all-reduce.4.cloned.1.call-start
  85.6 40.2 %all-gather.2.cloned.1.call-done = bf16[4096,128]{1,0:T(8,128)(2,1)} async-done(((bf16[512,128]{1,0:T(8,128)(2,1)}), bf16[4096,128]{1,0:T(8,128)(2,1)}) %all-gather.2.cloned.1.call-update) | async-done | bytes 1048592 | tf_op jit(solution)/shard_map/all_gather | solution.py:29
  125.8 4.7 %convolution_bitcast_fusion = f32[512,128]{0,1:T(8,128)} fusion(bf16[4096,128]{1,0:T(8,128)(2,1)} %all-gather.2.cloned.1.call-done, bf16[512,4096]{1,0:T(8,128)(2,1)} %param.2), kind=kOutput, calls=%fused_computation.1 | convolution fusion | flops 536870912 | bytes 5505024 | tf_op jit(solution)/shard_map/dot_general | solution.py:27
  130.6 0.0 all-reduce.4.cloned.1.call-update
  130.6 0.0 all-reduce.6.cloned.1.call-start
  130.6 17.1 %all-reduce.4.cloned.1.call-done = f32[512,128]{0,1:T(8,128)} async-done(((f32[512,128]{0,1:T(8,128)}), f32[512,128]{0,1:T(8,128)}) %all-reduce.4.cloned.1.call-update) | async-done | bytes 262160 | tf_op jit(solution)/shard_map/psum | solution.py:32
  147.8 2.0 fusion.1
  149.8 0.0 all-reduce.6.cloned.1.call-update
  149.8 0.0 all-reduce.8.cloned.1.call-start
  149.9 71.8 %all-reduce.6.cloned.1.call-done = f32[128,128]{0,1:T(8,128)} async-done(((f32[128,128]{0,1:T(8,128)}), f32[128,128]{0,1:T(8,128)}) %all-reduce.6.cloned.1.call-update) | async-done | bytes 65552 | tf_op jit(solution)/shard_map/psum | solution.py:36
  221.7 0.9 copy.5
  222.6 0.9 fusion.9
  223.5 11.7 %cholesky.16 = f32[128,128]{1,0:T(8,128)S(1)} custom-call(f32[128,128]{1,0:T(8,128)S(1)} %fusion.9), custom_call_target="Cholesky" | custom-call | tf_op jit(solution)/shard_map/jit(cholesky)/cholesky | solution.py:37
  235.2 0.6 compare_reduce_fusion
  235.8 0.7 fusion.7
  236.5 9.8 %custom-call.7 = f32[1,128,128]{1,2,0:T(8,128)S(1)} custom-call(f32[1,128,128]{2,1,0:T(8,128)S(1)} %fusion.7), custom_call_target="InvertDiagBlocksLowerTriangular" | custom-call | tf_op jit(solution)/shard_map/jit(_solve_triangular)/triangular_solve | solution.py:38
  246.3 1.5 convolution_multiply_fusion
  247.9 0.0 copy-start.1
  247.9 4.3 %fusion.3 = f32[128,4096]{1,0:T(8,128)} fusion(bf16[512,4096]{1,0:T(8,128)(2,1)} %param.2, f32[512,128]{1,0:T(8,128)S(1)} %convolution_multiply_fusion), kind=kOutput, calls=%fused_computation.7 | convolution fusion | flops 536936448 | bytes 6553600 | tf_op jit(solution)/shard_map/dot_general | solution.py:42
  252.2 0.0 all-reduce.8.cloned.1.call-update
  252.2 0.0 copy-done.1
  252.2 102.0 %all-reduce.8.cloned.1.call-done = f32[128,4096]{1,0:T(8,128)} async-done(((f32[128,4096]{1,0:T(8,128)}), f32[128,4096]{1,0:T(8,128)}) %all-reduce.8.cloned.1.call-update) | async-done | bytes 2097168 | tf_op jit(solution)/shard_map/psum | solution.py:45
  354.2 1.7 dynamic-slice_multiply_fusion
  (1 shorter events, 0.0 us)
Async XLA Ops:
  7.2 0.9 copy-start
  7.2 76.7 %reduce-scatter.2.cloned.1.call-start = ((), (), s32[]{:S(2)}) async-start(), calls=%async_computation.1 | async-start | bytes 2359296 | tf_op jit(solution)/shard_map/reduce_scatter | solution.py:17
  12.9 112.9 %all-gather.2.cloned.1.call-start = ((), (), s32[]{:S(2)}) async-start(), calls=%async_computation.2 | async-start | bytes 1179648 | tf_op jit(solution)/shard_map/all_gather | solution.py:29
  85.6 62.2 %all-reduce.4.cloned.1.call-start = ((), (), s32[]{:S(2)}) async-start(), calls=%async_computation.3 | async-start | bytes 524288 | tf_op jit(solution)/shard_map/psum | solution.py:32
  130.6 91.1 %all-reduce.6.cloned.1.call-start = ((), (), s32[]{:S(2)}) async-start(), calls=%async_computation.4 | async-start | bytes 131072 | tf_op jit(solution)/shard_map/psum | solution.py:36
  149.8 204.4 %all-reduce.8.cloned.1.call-start = ((), (), s32[]{:S(2)}) async-start(), calls=%async_computation.5 | async-start | bytes 4194304 | tf_op jit(solution)/shard_map/psum | solution.py:45
  247.9 4.4 %copy-start.1 = (f32[512,128]{1,0:T(8,128)}, f32[512,128]{1,0:T(8,128)S(1)}, u32[]{:S(2)}) copy-start(f32[512,128]{1,0:T(8,128)S(1)} %convolution_multiply_fusion) | copy-start | bytes 786436
Sparse Core Ops, SparseCore 0:
  13.0 70.8 reduce-scatter.1
  86.6 39.1 all-gather.1
  130.7 17.0 all-reduce.3
  152.0 69.6 all-reduce.5
  252.3 101.8 all-reduce.7
where the time goes:
time: 363 us; the launch traced here: 362 us
  waiting for transfers between devices  302 us (83%)
  other arithmetic  27 us (7%)
  matrix products  17.5 us (5%)
  between operations  13.8 us (4%)
    psum x1, waiting for transfers between devices, per_device(): summed = lax.psum(local_proj, 'row')  102 us
    psum x1, waiting for transfers between devices, per_device(): gram = lax.psum(local_gram, 'row')  71.8 us
    reduce_scatter x1, waiting for transfers between devices, per_device(): lax.psum_scatter(lax.dot_general(block, start_sketch, (((0,), (0,)), ((),...  70.9 us
    all_gather x1, waiting for transfers between devices, per_device(): lax.all_gather(sketch_cols, 'row', axis=0, tiled=True)  40.2 us
    psum x1, waiting for transfers between devices, per_device(): sketch = lax.psum(partial_sketch, 'col') / total_cols  17.1 us
    another operation x3, other arithmetic, per_device(): factor = jnp.linalg.cholesky(gram)  12.4 us
    another operation x2, other arithmetic, per_device(): solved = jax.scipy.linalg.solve_triangular(factor, sketch.T, lower=True)  10.5 us
  transfers between devices with their start and end apart: 5, of which 5 were waited for; matrix products, arithmetic and copies ran while one was open for 0% of the time, Pallas kernels for 0%

commit v1 on v0

v1 whole, which is shorter than its diff:
```python
import math

import jax
import jax.numpy as jnp
from jax import lax
from jax.sharding import PartitionSpec as P


def exchange_sum(value, axis):
    size = lax.axis_size(axis)
    step = 1
    while step < size:
        pairs = [(i, i ^ step) for i in range(size)]
        value = value + lax.ppermute(value, axis, pairs)
        step *= 2
    return value


def scatter_sum(blocks, axis):
    landed = lax.all_to_all(blocks.astype(jnp.bfloat16), axis, 0, 0, tiled=True)
    return jnp.sum(landed.astype(jnp.float32), axis=0)


def gather(block, axis):
    copies = jnp.broadcast_to(block[None], (lax.axis_size(axis),) + block.shape)
    return lax.all_to_all(copies, axis, 0, 0, tiled=True)


def per_device(activations, start_sketch):
    rows_here, cols_here = activations.shape
    width = start_sketch.shape[1]
    parts = lax.axis_size("row")
    total_rows = rows_here * parts
    total_cols = cols_here * lax.axis_size("col")
    root_rows = math.sqrt(total_rows)

    local_cols = lax.dot_general(
        activations, start_sketch, (((0,), (0,)), ((), ())), preferred_element_type=jnp.float32
    )
    share = scatter_sum(local_cols.reshape(parts, cols_here // parts, width), "row")
    sketch_cols = gather((share / root_rows).astype(jnp.bfloat16), "row").reshape(cols_here, width)

    partial_sketch = jnp.dot(activations, sketch_cols, preferred_element_type=jnp.float32)
    sketch = exchange_sum(partial_sketch, "col") / total_cols

    local_gram = lax.dot_general(
        sketch, sketch, (((0,), (0,)), ((), ())), precision=lax.Precision.HIGHEST
    )
    gram = exchange_sum(local_gram, "row")
    factor = jnp.linalg.cholesky(gram)
    solved = jax.scipy.linalg.solve_triangular(factor, sketch.T, lower=True)
    basis = solved.T * root_rows

    high = basis.astype(jnp.bfloat16)
    low = (basis - high.astype(jnp.float32)).astype(jnp.bfloat16)
    pair = jnp.concatenate([high, low], axis=1)
    local_pair = lax.dot_general(
        pair, activations, (((0,), (0,)), ((), ())), preferred_element_type=jnp.float32
    )
    local_proj = local_pair[:width] + local_pair[width:]
    projection = (
        scatter_sum(local_proj.reshape(parts, width // parts, cols_here), "row") / total_rows
    )
    return (basis, projection)


def solution(mesh):
    return jax.shard_map(
        per_device,
        mesh=mesh,
        in_specs=(P(("grp", "row"), "col"), P(("grp", "row"), None)),
        out_specs=(P(("grp", "row"), None), P(("grp", "row"), "col")),
        check_vma=False,
    )
```

time: 363 us -> 141 us (0.39)
  waiting for transfers between devices: 302 us -> 34.6 us
  blocking collectives: 0 us -> 61.9 us
  between operations: 13.8 us -> 0.76 us
  matrix products: 17.5 us -> 9.27 us
  starting transfers between devices: 0.21 us -> 7.32 us
    psum x3 -> x0, waiting for transfers between devices: 191 us -> none  [the longest x1 102 us: per_device(): summed = lax.psum(local_proj, 'row')]
    reduce_scatter x1 -> x0, waiting for transfers between devices: 70.9 us -> none  [per_device(): lax.psum_scatter(lax.dot_general(block, start_sketch, (((0,), (0,)), ((),...]
    all_to_all x0 -> x2, blocking collectives: none -> 61.9 us  [the longest x1 33.1 us: scatter_sum(): landed = lax.all_to_all(blocks.astype(jnp.bfloat16), axis, 0, 0, tiled=True)]
    all_gather x1 -> x0, waiting for transfers between devices: 40.2 us -> none  [per_device(): lax.all_gather(sketch_cols, 'row', axis=0, tiled=True)]
    all_to_all x0 -> x1, waiting for transfers between devices: none -> 22.2 us  [scatter_sum(): landed = lax.all_to_all(blocks.astype(jnp.bfloat16), axis, 0, 0, tiled=True)]
    ppermute x0 -> x4, waiting for transfers between devices: none -> 12.4 us  [exchange_sum(): value = value + lax.ppermute(value, axis, pairs)]
    dot_general x3, matrix products: 13.9 us -> 8.46 us  [the longest x1 3.5 us: per_device(): lax.dot_general(activations, start_sketch, (((0,), (0,)), ((), ())), pref...]
    ppermute x0 -> x4, starting transfers between devices: none -> 3.76 us  [exchange_sum(): value = value + lax.ppermute(value, axis, pairs)]
  transfers between devices with their start and end apart: 5 -> 5, of which waited for: 5 -> 5; matrix products, arithmetic and copies ran while one was open for 0% -> 1% of each run, Pallas kernels for 0% -> 0%
where the time goes in v1:
time: 141 us
  blocking collectives  61.9 us (44%)
  waiting for transfers between devices  34.6 us (25%)
  other arithmetic  25.1 us (18%)
  matrix products  9.27 us (7%)
  starting transfers between devices  7.32 us (5%)
  local copies, waits for them, and re-layouts  1.97 us (1%)
    all_to_all x1, blocking collectives, scatter_sum(): landed = lax.all_to_all(blocks.astype(jnp.bfloat16), axis, 0, 0, tiled=True)  33.1 us
    all_to_all x1, blocking collectives, gather(): return lax.all_to_all(copies, axis, 0, 0, tiled=True)  28.8 us
    all_to_all x1, waiting for transfers between devices, scatter_sum(): landed = lax.all_to_all(blocks.astype(jnp.bfloat16), axis, 0, 0, tiled=True)  22.2 us
    ppermute x4, waiting for transfers between devices, exchange_sum(): value = value + lax.ppermute(value, axis, pairs)  12.4 us
    another operation x3, other arithmetic, per_device(): factor = jnp.linalg.cholesky(gram)  12.4 us
    another operation x2, other arithmetic, per_device(): solved = jax.scipy.linalg.solve_triangular(factor, sketch.T, lower=True)  10.5 us
    ppermute x4, starting transfers between devices, exchange_sum(): value = value + lax.ppermute(value, axis, pairs)  3.76 us
    all_to_all x1, starting transfers between devices, scatter_sum(): landed = lax.all_to_all(blocks.astype(jnp.bfloat16), axis, 0, 0, tiled=True)  3.56 us
  transfers between devices with their start and end apart: 5, of which 5 were waited for; matrix products, arithmetic and copies ran while one was open for 1% of the time, Pallas kernels for 0%

profile of v1, /device:TPU:0, one launch (start us, length us, event | category | flops | bytes accessed | tf_op | source)
XLA Modules:
  0.0 141.0 jit_solution(4993351041303964628)
XLA Ops:
  0.6 0.0 copy-start
  0.6 0.9 copy-done
  1.5 3.5 %convolution_convert_fusion = bf16[4096,128]{1,0:T(8,128)(2,1)S(1)} fusion(bf16[512,4096]{1,0:T(8,128)(2,1)} %param.2, bf16[512,128]{1,0:T(8,128)(2,1)S(1)} %copy-done), kind=kOutput, calls=%fused_computation | convolution fusion | flops 537395200 | bytes 5373952 | tf_op jit(solution)/shard_map/dot_general | solution.py:37
  5.0 0.0 copy-start.1
  5.1 33.1 %all_to_all.15 = bf16[8,512,128]{2,1,0:T(8,128)(2,1)S(1)} all-to-all(bf16[8,512,128]{2,1,0:T(8,128)(2,1)S(1)} %bitcast.21), channel_id=1, replica_groups=mesh['grp'=2,'row'=8,'col'=2] {'row'}, dimensions={0} | all-to-all | bytes 2097152 | tf_op jit(solution)/shard_map/all_to_all | solution.py:20
  38.1 0.1 convert_reduce_fusion.1
  38.3 0.1 broadcast_in_dim.3
  38.5 28.8 %all_to_all.16 = bf16[8,512,128]{2,1,0:T(8,128)(2,1)S(1)} all-to-all(bf16[8,512,128]{2,1,0:T(8,128)(2,1)S(1)} %broadcast_in_dim.3), channel_id=1, replica_groups=mesh['grp'=2,'row'=8,'col'=2] {'row'}, dimensions={0} | all-to-all | bytes 2097152 | tf_op jit(solution)/shard_map/all_to_all | solution.py:26
  67.3 0.0 copy-done.1
  67.3 1.5 %convolution_bitcast_fusion = f32[512,128]{0,1:T(8,128)S(1)} fusion(bf16[4096,128]{1,0:T(8,128)(2,1)S(1)} %bitcast.22, bf16[512,4096]{1,0:T(8,128)(2,1)S(1)} %copy-done.1), kind=kOutput, calls=%fused_computation.6 | convolution fusion | flops 536870912 | bytes 5505024 | tf_op jit(solution)/shard_map/dot_general | solution.py:43
  68.8 0.1 collective-permute-start
  68.9 1.5 %collective-permute-done = f32[512,128]{0,1:T(8,128)S(1)} collective-permute-done((f32[512,128]{0,1:T(8,128)S(1)}, f32[512,128]{0,1:T(8,128)S(1)}, u32[]{:S(2)}, u32[]{:S(2)}) %collective-permute-start) | collective-permute-done | bytes 262176 | tf_op jit(solution)/shard_map/ppermute | solution.py:14
  70.4 0.4 fusion.5
  70.8 1.5 %collective-permute-start.1 = (f32[128,128]{0,1:T(8,128)S(1)}, f32[128,128]{0,1:T(8,128)S(1)}, u32[]{:S(2)}, u32[]{:S(2)}) collective-permute-start(f32[128,128]{0,1:T(8,128)S(1)} %fusion.5), channel_id=1, source_target_pairs={{0,2},{2,0},{4,6},{6,4},{8,10},{10,8},{12,14},{14,12},{1,3},{3,1},... | collective-permute-start | bytes 196616 | tf_op jit(solution)/shard_map/ppermute | solution.py:14
  72.3 2.9 %collective-permute-done.1 = f32[128,128]{0,1:T(8,128)S(1)} collective-permute-done((f32[128,128]{0,1:T(8,128)S(1)}, f32[128,128]{0,1:T(8,128)S(1)}, u32[]{:S(2)}, u32[]{:S(2)}) %collective-permute-start.1) | collective-permute-done | bytes 65568 | tf_op jit(solution)/shard_map/ppermute | solution.py:14
  75.2 1.1 collective-permute-start.2
  76.3 3.2 %collective-permute-done.2 = f32[128,128]{0,1:T(8,128)S(1)} collective-permute-done((f32[128,128]{0,1:T(8,128)S(1)}, f32[128,128]{0,1:T(8,128)S(1)}, u32[]{:S(2)}, u32[]{:S(2)}) %collective-permute-start.2) | collective-permute-done | bytes 65568 | tf_op jit(solution)/shard_map/ppermute | solution.py:14
  79.5 1.1 collective-permute-start.3
  80.6 4.8 %collective-permute-done.3 = f32[128,128]{0,1:T(8,128)S(1)} collective-permute-done((f32[128,128]{0,1:T(8,128)S(1)}, f32[128,128]{0,1:T(8,128)S(1)}, u32[]{:S(2)}, u32[]{:S(2)}) %collective-permute-start.3) | collective-permute-done | bytes 65568 | tf_op jit(solution)/shard_map/ppermute | solution.py:14
  85.5 0.1 copy.6
  85.6 11.7 %cholesky.16 = f32[128,128]{1,0:T(8,128)S(1)} custom-call(f32[128,128]{1,0:T(8,128)S(1)} %fusion.8), custom_call_target="Cholesky" | custom-call | tf_op jit(solution)/shard_map/jit(cholesky)/cholesky | solution.py:50
  97.3 0.6 compare_reduce_fusion
  98.0 0.7 fusion.6
  98.6 9.8 %custom-call.7 = f32[1,128,128]{1,2,0:T(8,128)S(1)} custom-call(f32[1,128,128]{2,1,0:T(8,128)S(1)} %fusion.6), custom_call_target="InvertDiagBlocksLowerTriangular" | custom-call | tf_op jit(solution)/shard_map/jit(_solve_triangular)/triangular_solve | solution.py:51
  108.5 0.4 subtract_convert_fusion
  108.9 3.4 %fusion.1 = f32[256,4096]{1,0:T(8,128)S(1)} fusion(bf16[512,4096]{1,0:T(8,128)(2,1)} %param.2, bf16[512,128]{0,1:T(8,128)(2,1)S(1)} %get-tuple-element.4, bf16[512,128]{0,1:T(8,128)(2,1)S(1)} %get-tuple-element.5), kind=kOutput, calls=%fused_computation.7 | convolution fusion | flops 1074266112 | bytes 8650752 | tf_op jit(solution)/shard_map/dot_general | solution.py:57
  112.3 1.2 fusion
  113.5 3.6 %all-to-all-start.2 = ((bf16[8,16,4096]{2,1,0:T(8,128)(2,1)}), bf16[8,16,4096]{2,1,0:T(8,128)(2,1)S(1)}, u32[]{:S(2)}, u32[]{:S(2)}) async-start(bf16[8,16,4096]{2,1,0:T(8,128)(2,1)} %bitcast.6), calls=%async_computation.2 | async-start | bytes 2097152 | tf_op jit(solution)/shard_map/all_to_all | solution.py:20
  117.1 0.8 copy.7
  117.9 22.2 %all-to-all-done.2 = bf16[8,16,4096]{2,1,0:T(8,128)(2,1)S(1)} async-done(((bf16[8,16,4096]{2,1,0:T(8,128)(2,1)}), bf16[8,16,4096]{2,1,0:T(8,128)(2,1)S(1)}, u32[]{:S(2)}, u32[]{:S(2)}) %all-to-all-start.2) | async-done | bytes 1048608 | tf_op jit(solution)/shard_map/all_to_all | solution.py:20
  140.1 0.1 convert_reduce_fusion
  140.2 0.7 broadcast_multiply_fusion
  (6 shorter events, 0.1 us)
Async XLA Ops:
  0.6 0.9 copy-start
  5.0 62.3 %copy-start.1 = (bf16[512,4096]{1,0:T(8,128)(2,1)S(1)}, bf16[512,4096]{1,0:T(8,128)(2,1)}, u32[]{:S(2)}) copy-start(bf16[512,4096]{1,0:T(8,128)(2,1)} %param.2) | copy-start | bytes 12582916
  68.8 1.6 %collective-permute-start = (f32[512,128]{0,1:T(8,128)S(1)}, f32[512,128]{0,1:T(8,128)S(1)}, u32[]{:S(2)}, u32[]{:S(2)}) collective-permute-start(f32[512,128]{0,1:T(8,128)S(1)} %convolution_bitcast_fusion), channel_id=1, source_target_pairs={{0,1},{1,0},{2,3},{3,2},{4,5},{5,4},{6,7},{7,6},{8,9},{9,8},{10,11... | collective-permute-start | bytes 786440 | tf_op jit(solution)/shard_map/ppermute | solution.py:14
  70.8 4.3 %collective-permute-start.1 = (f32[128,128]{0,1:T(8,128)S(1)}, f32[128,128]{0,1:T(8,128)S(1)}, u32[]{:S(2)}, u32[]{:S(2)}) collective-permute-start(f32[128,128]{0,1:T(8,128)S(1)} %fusion.5), channel_id=1, source_target_pairs={{0,2},{2,0},{4,6},{6,4},{8,10},{10,8},{12,14},{14,12},{1,3},{3,1},... | collective-permute-start | bytes 196616 | tf_op jit(solution)/shard_map/ppermute | solution.py:14
  75.2 4.3 %collective-permute-start.2 = (f32[128,128]{0,1:T(8,128)S(1)}, f32[128,128]{0,1:T(8,128)S(1)}, u32[]{:S(2)}, u32[]{:S(2)}) collective-permute-start(f32[128,128]{0,1:T(8,128)S(1)} %add.28), channel_id=1, source_target_pairs={{0,4},{2,6},{4,0},{6,2},{8,12},{10,14},{12,8},{14,10},{1,5},{3,7},... | collective-permute-start | bytes 196616 | tf_op jit(solution)/shard_map/ppermute | solution.py:14
  79.5 5.9 %collective-permute-start.3 = (f32[128,128]{0,1:T(8,128)S(1)}, f32[128,128]{0,1:T(8,128)S(1)}, u32[]{:S(2)}, u32[]{:S(2)}) collective-permute-start(f32[128,128]{0,1:T(8,128)S(1)} %add.29), channel_id=1, source_target_pairs={{0,8},{2,10},{4,12},{6,14},{8,0},{10,2},{12,4},{14,6},{1,9},{3,11}... | collective-permute-start | bytes 196616 | tf_op jit(solution)/shard_map/ppermute | solution.py:14
  113.5 26.6 %all-to-all-start.2 = ((bf16[8,16,4096]{2,1,0:T(8,128)(2,1)}), bf16[8,16,4096]{2,1,0:T(8,128)(2,1)S(1)}, u32[]{:S(2)}, u32[]{:S(2)}) async-start(bf16[8,16,4096]{2,1,0:T(8,128)(2,1)} %bitcast.6), calls=%async_computation.2 | async-start | bytes 2097152 | tf_op jit(solution)/shard_map/all_to_all | solution.py:20

commit v2 on v1

v2 whole, which is shorter than its diff:
```python
import math

import jax
import jax.numpy as jnp
from jax import lax
from jax.sharding import PartitionSpec as P

CHUNKS = 2


def levels_of(size):
    levels, stride = [], 1
    while stride < size:
        radix = 2 if stride == 1 else min(4, size // stride)
        levels.append((stride, radix))
        stride *= radix
    return levels


def swap(value, axis, distance):
    size = lax.axis_size(axis)
    return lax.ppermute(value, axis, [(i, i ^ distance) for i in range(size)])


def exchange_sum(value, axis):
    step = 1
    while step < lax.axis_size(axis):
        value = value + swap(value, axis, step)
        step *= 2
    return value


def digit_of(axis, stride, radix):
    return lax.rem(lax.div(lax.axis_index(axis), stride), radix)


def scatter_level(blocks, axis, stride, radix):
    digit = digit_of(axis, stride, radix)
    view = blocks.reshape((blocks.shape[0] // radix, radix) + blocks.shape[1:])
    total = lax.dynamic_index_in_dim(view, digit, 1, keepdims=False)
    for t in range(1, radix):
        part = lax.dynamic_index_in_dim(view, jnp.bitwise_xor(digit, t), 1, keepdims=False)
        landed = swap(part.astype(jnp.bfloat16), axis, t * stride)
        total = total + landed.astype(jnp.float32)
    return total


def scatter_sum(blocks, axis):
    for stride, radix in levels_of(lax.axis_size(axis)):
        blocks = scatter_level(blocks, axis, stride, radix)
    return blocks[0]


def gather_level(blocks, axis, stride, radix):
    digit = digit_of(axis, stride, radix)
    held = [blocks] + [swap(blocks, axis, t * stride) for t in range(1, radix)]
    bit = 1
    while bit < radix:
        flip = jnp.bitwise_and(digit, bit) != 0
        held = [jnp.where(flip, held[j ^ bit], held[j]) for j in range(radix)]
        bit *= 2
    whole = jnp.stack(held, axis=1)
    return whole.reshape((blocks.shape[0] * radix,) + blocks.shape[1:])


def gather(block, axis):
    blocks = block[None]
    for stride, radix in reversed(levels_of(lax.axis_size(axis))):
        blocks = gather_level(blocks, axis, stride, radix)
    return blocks


def per_device(activations, start_sketch):
    rows_here, cols_here = activations.shape
    width = start_sketch.shape[1]
    parts = lax.axis_size("row")
    total_rows = rows_here * parts
    total_cols = cols_here * lax.axis_size("col")
    root_rows = math.sqrt(total_rows)

    cols_chunk = cols_here // CHUNKS
    spans = [slice(c * cols_chunk, (c + 1) * cols_chunk) for c in range(CHUNKS)]

    partial_sketch = 0.0
    for span in spans:
        local_cols = lax.dot_general(
            activations[:, span],
            start_sketch,
            (((0,), (0,)), ((), ())),
            preferred_element_type=jnp.float32,
        )
        share = scatter_sum(local_cols.reshape(parts, cols_chunk // parts, width), "row")
        chunk = gather((share / root_rows).astype(jnp.bfloat16), "row")
        partial_sketch = partial_sketch + jnp.dot(
            activations[:, span],
            chunk.reshape(cols_chunk, width),
            preferred_element_type=jnp.float32,
        )
    sketch = exchange_sum(partial_sketch, "col") / total_cols

    local_gram = lax.dot_general(
        sketch, sketch, (((0,), (0,)), ((), ())), precision=lax.Precision.HIGHEST
    )
    gram = exchange_sum(local_gram, "row")
    factor = jnp.linalg.cholesky(gram)
    solved = jax.scipy.linalg.solve_triangular(factor, sketch.T, lower=True)
    basis = solved.T * root_rows

    high = basis.astype(jnp.bfloat16)
    low = (basis - high.astype(jnp.float32)).astype(jnp.bfloat16)
    pair = jnp.concatenate([high, low], axis=1)
    pieces = []
    for span in spans:
        local_pair = lax.dot_general(
            pair, activations[:, span], (((0,), (0,)), ((), ())), preferred_element_type=jnp.float32
        )
        local_proj = local_pair[:width] + local_pair[width:]
        pieces.append(
            scatter_sum(local_proj.reshape(parts, width // parts, cols_chunk), "row") / total_rows
        )
    return (basis, jnp.concatenate(pieces, axis=1))


def solution(mesh):
    return jax.shard_map(
        per_device,
        mesh=mesh,
        in_specs=(P(("grp", "row"), "col"), P(("grp", "row"), None)),
        out_specs=(P(("grp", "row"), None), P(("grp", "row"), "col")),
        check_vma=False,
    )
```

time: 141 us -> 115 us (0.82)
  blocking collectives: 61.9 us -> 0 us
  starting transfers between devices: 7.32 us -> 36.7 us
  waiting for transfers between devices: 34.6 us -> 39.5 us
    all_to_all x2 -> x0, blocking collectives: 61.9 us -> none  [the longest x1 33.1 us: scatter_sum(): landed = lax.all_to_all(blocks.astype(jnp.bfloat16), axis, 0, 0, tiled=True)]
    ppermute x4 -> x28, starting transfers between devices: 3.76 us -> 36.7 us  [swap(): return lax.ppermute(value, axis, [(i, i ^ distance) for i in range(size)])]
    ppermute x4 -> x28, waiting for transfers between devices: 12.4 us -> 39.5 us  [swap(): return lax.ppermute(value, axis, [(i, i ^ distance) for i in range(size)])]
    all_to_all x1 -> x0, waiting for transfers between devices: 22.2 us -> none  [scatter_sum(): landed = lax.all_to_all(blocks.astype(jnp.bfloat16), axis, 0, 0, tiled=True)]
    all_to_all x1 -> x0, starting transfers between devices: 3.56 us -> none  [scatter_sum(): landed = lax.all_to_all(blocks.astype(jnp.bfloat16), axis, 0, 0, tiled=True)]
    dot_general x3 -> x6, matrix products: 8.46 us -> 9.5 us  [the longest x2 4.65 us: per_device(): lax.dot_general(activations[:, span], start_sketch, (((0,), (0,)), ((), (...]
  transfers between devices with their start and end apart: 5 -> 28, of which waited for: 5 -> 16; matrix products, arithmetic and copies ran while one was open for 1% -> 4% of each run, Pallas kernels for 0% -> 0%
where the time goes in v2:
time: 115 us; the launch traced here: 114 us
  waiting for transfers between devices  39.5 us (34%)
  starting transfers between devices  36.7 us (32%)
  other arithmetic  24.5 us (21%)
  matrix products  10.3 us (9%)
  local copies, waits for them, and re-layouts  2.48 us (2%)
    ppermute x28, waiting for transfers between devices, swap(): return lax.ppermute(value, axis, [(i, i ^ distance) for i in range(size)])  39.5 us
    ppermute x28, starting transfers between devices, swap(): return lax.ppermute(value, axis, [(i, i ^ distance) for i in range(size)])  36.7 us
    another operation x3, other arithmetic, per_device(): factor = jnp.linalg.cholesky(gram)  12.4 us
    another operation x2, other arithmetic, per_device(): solved = jax.scipy.linalg.solve_triangular(factor, sketch.T, lower=True)  10.5 us
    dot_general x2, matrix products, per_device(): lax.dot_general(activations[:, span], start_sketch, (((0,), (0,)), ((), (...  4.65 us
    dot_general x2, matrix products, per_device(): lax.dot_general(pair, activations[:, span], (((0,), (0,)), ((), ())), pre...  3.18 us
  transfers between devices with their start and end apart: 28, of which 16 were waited for; matrix products, arithmetic and copies ran while one was open for 4% of the time, Pallas kernels for 0%

profile of v2, /device:TPU:0, one launch (start us, length us, event | category | flops | bytes accessed | tf_op | source)
XLA Modules:
  0.0 114.5 jit_solution(11854347509041918215)
XLA Ops:
  0.7 0.9 copy-done
  1.5 2.3 %fusion.4 = f32[2048,128]{1,0:T(8,128)S(1)} fusion(bf16[512,128]{1,0:T(8,128)(2,1)S(1)} %copy-done, bf16[512,4096]{1,0:T(8,128)(2,1)} %param.2), kind=kOutput, calls=%fused_computation.4 | convolution fusion | flops 268435456 | bytes 3276800 | tf_op jit(solution)/shard_map/dot_general | solution.py:86
  3.9 3.0 %collective-permute-start.8 = (bf16[4,256,128]{2,1,0:T(8,128)(2,1)S(1)}, bf16[4,256,128]{2,1,0:T(8,128)(2,1)S(1)}, u32[]{:S(2)}, u32[]{:S(2)}) collective-permute-start(bf16[4,256,128]{2,1,0:T(8,128)(2,1)S(1)} %fusion.19), channel_id=1, source_target_pairs={{0,2},{2,0},{4,6},{6,4},{8,10},{10,8},{12,14},{14,12},{1,3},{3,1},... | collective-permute-start | bytes 786440 | tf_op jit(solution)/shard_map/ppermute | solution.py:22
  6.9 2.3 %fusion.10 = f32[2048,128]{1,0:T(8,128)S(1)} fusion(bf16[512,128]{1,0:T(8,128)(2,1)S(1)} %copy-done, bf16[512,4096]{1,0:T(8,128)(2,1)} %param.2), kind=kOutput, calls=%fused_computation.10 | convolution fusion | flops 268435456 | bytes 3276800 | tf_op jit(solution)/shard_map/dot_general | solution.py:86
  9.4 4.6 %collective-permute-done.8 = bf16[4,256,128]{2,1,0:T(8,128)(2,1)S(1)} collective-permute-done((bf16[4,256,128]{2,1,0:T(8,128)(2,1)S(1)}, bf16[4,256,128]{2,1,0:T(8,128)(2,1)S(1)}, u32[]{:S(2)}, u32[]{:S(2)}) %collective-permute-start.8) | collective-permute-done | bytes 262176 | tf_op jit(solution)/shard_map/ppermute | solution.py:22
  14.2 2.2 %collective-permute-start.9 = (bf16[1,256,128]{2,1,0:T(8,128)(2,1)S(1)}, bf16[1,256,128]{2,1,0:T(8,128)(2,1)S(1)}, u32[]{:S(2)}, u32[]{:S(2)}) collective-permute-start(bf16[1,256,128]{2,1,0:T(8,128)(2,1)S(1)} %get-tuple-element.19), channel_id=1, source_target_pairs={{0,4},{2,6},{4,0},{6,2},{8,12},{10,14},{12,8},{14,10},{1,5},{3,7},... | collective-permute-start | bytes 196616 | tf_op jit(solution)/shard_map/ppermute | solution.py:22
  16.4 2.5 %collective-permute-start.11 = (bf16[1,256,128]{2,1,0:T(8,128)(2,1)S(1)}, bf16[1,256,128]{2,1,0:T(8,128)(2,1)S(1)}, u32[]{:S(2)}, u32[]{:S(2)}) collective-permute-start(bf16[1,256,128]{2,1,0:T(8,128)(2,1)S(1)} %get-tuple-element.20), channel_id=1, source_target_pairs={{0,12},{2,14},{4,8},{6,10},{8,4},{10,6},{12,0},{14,2},{1,13},{3,15... | collective-permute-start | bytes 196616 | tf_op jit(solution)/shard_map/ppermute | solution.py:22
  19.1 1.9 %collective-permute-start.1 = (bf16[1,256,128]{2,1,0:T(8,128)(2,1)S(1)}, bf16[1,256,128]{2,1,0:T(8,128)(2,1)S(1)}, u32[]{:S(2)}, u32[]{:S(2)}) collective-permute-start(bf16[1,256,128]{2,1,0:T(8,128)(2,1)S(1)} %get-tuple-element.14), channel_id=1, source_target_pairs={{0,4},{2,6},{4,0},{6,2},{8,12},{10,14},{12,8},{14,10},{1,5},{3,7},... | collective-permute-start | bytes 196616 | tf_op jit(solution)/shard_map/ppermute | solution.py:22
  20.9 2.5 %collective-permute-start.3 = (bf16[1,256,128]{2,1,0:T(8,128)(2,1)S(1)}, bf16[1,256,128]{2,1,0:T(8,128)(2,1)S(1)}, u32[]{:S(2)}, u32[]{:S(2)}) collective-permute-start(bf16[1,256,128]{2,1,0:T(8,128)(2,1)S(1)} %get-tuple-element.15), channel_id=1, source_target_pairs={{0,12},{2,14},{4,8},{6,10},{8,4},{10,6},{12,0},{14,2},{1,13},{3,15... | collective-permute-start | bytes 196616 | tf_op jit(solution)/shard_map/ppermute | solution.py:22
  23.4 3.8 %collective-permute-done.10 = bf16[1,256,128]{2,1,0:T(8,128)(2,1)S(1)} collective-permute-done((bf16[1,256,128]{2,1,0:T(8,128)(2,1)S(1)}, bf16[1,256,128]{2,1,0:T(8,128)(2,1)S(1)}, u32[]{:S(2)}, u32[]{:S(2)}) %collective-permute-start.10) | collective-permute-done | bytes 65568 | tf_op jit(solution)/shard_map/ppermute | solution.py:22
  27.8 4.0 %collective-permute-start.12 = (bf16[1,256,128]{2,1,0:T(8,128)(2,1)S(1)}, bf16[1,256,128]{2,1,0:T(8,128)(2,1)S(1)}, u32[]{:S(2)}, u32[]{:S(2)}) collective-permute-start(bf16[1,256,128]{2,1,0:T(8,128)(2,1)S(1)} %multiply_convert_fusion), channel_id=1, source_target_pairs={{0,12},{2,14},{4,8},{6,10},{8,4},{10,6},{12,0},{14,2},{1,13},{3,15... | collective-permute-start | bytes 196616 | tf_op jit(solution)/shard_map/ppermute | solution.py:22
  31.8 0.6 collective-permute-done.2
  32.5 3.0 %collective-permute-start.5 = (bf16[1,256,128]{2,1,0:T(8,128)(2,1)S(1)}, bf16[1,256,128]{2,1,0:T(8,128)(2,1)S(1)}, u32[]{:S(2)}, u32[]{:S(2)}) collective-permute-start(bf16[1,256,128]{2,1,0:T(8,128)(2,1)S(1)} %multiply_convert_fusion.1), channel_id=1, source_target_pairs={{0,8},{2,10},{4,12},{6,14},{8,0},{10,2},{12,4},{14,6},{1,9},{3,11}... | collective-permute-start | bytes 196616 | tf_op jit(solution)/shard_map/ppermute | solution.py:22
  35.5 1.4 %collective-permute-start.4 = (bf16[1,256,128]{2,1,0:T(8,128)(2,1)S(1)}, bf16[1,256,128]{2,1,0:T(8,128)(2,1)S(1)}, u32[]{:S(2)}, u32[]{:S(2)}) collective-permute-start(bf16[1,256,128]{2,1,0:T(8,128)(2,1)S(1)} %multiply_convert_fusion.1), channel_id=1, source_target_pairs={{0,12},{2,14},{4,8},{6,10},{8,4},{10,6},{12,0},{14,2},{1,13},{3,15... | collective-permute-start | bytes 196616 | tf_op jit(solution)/shard_map/ppermute | solution.py:22
  36.9 1.6 %collective-permute-start.15 = (bf16[4,256,128]{2,1,0:T(8,128)(2,1)S(1)}, bf16[4,256,128]{2,1,0:T(8,128)(2,1)S(1)}, u32[]{:S(2)}, u32[]{:S(2)}) collective-permute-start(bf16[4,256,128]{2,1,0:T(8,128)(2,1)S(1)} %maximum_bitcast_fusion.1), channel_id=1, source_target_pairs={{0,2},{2,0},{4,6},{6,4},{8,10},{10,8},{12,14},{14,12},{1,3},{3,1},... | collective-permute-start | bytes 786440 | tf_op jit(solution)/shard_map/ppermute | solution.py:22
  38.5 1.3 %collective-permute-done.5 = bf16[1,256,128]{2,1,0:T(8,128)(2,1)S(1)} collective-permute-done((bf16[1,256,128]{2,1,0:T(8,128)(2,1)S(1)}, bf16[1,256,128]{2,1,0:T(8,128)(2,1)S(1)}, u32[]{:S(2)}, u32[]{:S(2)}) %collective-permute-start.5) | collective-permute-done | bytes 65568 | tf_op jit(solution)/shard_map/ppermute | solution.py:22
  39.8 1.7 %collective-permute-done.4 = bf16[1,256,128]{2,1,0:T(8,128)(2,1)S(1)} collective-permute-done((bf16[1,256,128]{2,1,0:T(8,128)(2,1)S(1)}, bf16[1,256,128]{2,1,0:T(8,128)(2,1)S(1)}, u32[]{:S(2)}, u32[]{:S(2)}) %collective-permute-start.4) | collective-permute-done | bytes 65568 | tf_op jit(solution)/shard_map/ppermute | solution.py:22
  41.6 1.6 %collective-permute-start.7 = (bf16[4,256,128]{2,1,0:T(8,128)(2,1)S(1)}, bf16[4,256,128]{2,1,0:T(8,128)(2,1)S(1)}, u32[]{:S(2)}, u32[]{:S(2)}) collective-permute-start(bf16[4,256,128]{2,1,0:T(8,128)(2,1)S(1)} %maximum_bitcast_fusion), channel_id=1, source_target_pairs={{0,2},{2,0},{4,6},{6,4},{8,10},{10,8},{12,14},{14,12},{1,3},{3,1},... | collective-permute-start | bytes 786440 | tf_op jit(solution)/shard_map/ppermute | solution.py:22
  43.2 2.6 %collective-permute-done.15 = bf16[4,256,128]{2,1,0:T(8,128)(2,1)S(1)} collective-permute-done((bf16[4,256,128]{2,1,0:T(8,128)(2,1)S(1)}, bf16[4,256,128]{2,1,0:T(8,128)(2,1)S(1)}, u32[]{:S(2)}, u32[]{:S(2)}) %collective-permute-start.15) | collective-permute-done | bytes 262176 | tf_op jit(solution)/shard_map/ppermute | solution.py:22
  46.0 0.8 fusion.2
  46.8 2.2 %collective-permute-done.7 = bf16[4,256,128]{2,1,0:T(8,128)(2,1)S(1)} collective-permute-done((bf16[4,256,128]{2,1,0:T(8,128)(2,1)S(1)}, bf16[4,256,128]{2,1,0:T(8,128)(2,1)S(1)}, u32[]{:S(2)}, u32[]{:S(2)}) %collective-permute-start.7) | collective-permute-done | bytes 262176 | tf_op jit(solution)/shard_map/ppermute | solution.py:22
  49.1 0.8 fusion.15
  50.0 1.5 %collective-permute-done.16 = f32[512,128]{0,1:T(8,128)S(1)} collective-permute-done((f32[512,128]{0,1:T(8,128)S(1)}, f32[512,128]{0,1:T(8,128)S(1)}, u32[]{:S(2)}, u32[]{:S(2)}) %collective-permute-start.16) | collective-permute-done | bytes 262176 | tf_op jit(solution)/shard_map/ppermute | solution.py:22
  51.9 1.6 %collective-permute-start.17 = (f32[128,128]{0,1:T(8,128)S(1)}, f32[128,128]{0,1:T(8,128)S(1)}, u32[]{:S(2)}, u32[]{:S(2)}) collective-permute-start(f32[128,128]{0,1:T(8,128)S(1)} %fusion.22), channel_id=1, source_target_pairs={{0,2},{2,0},{4,6},{6,4},{8,10},{10,8},{12,14},{14,12},{1,3},{3,1},... | collective-permute-start | bytes 196616 | tf_op jit(solution)/shard_map/ppermute | solution.py:22
  53.5 2.8 %collective-permute-done.17 = f32[128,128]{0,1:T(8,128)S(1)} collective-permute-done((f32[128,128]{0,1:T(8,128)S(1)}, f32[128,128]{0,1:T(8,128)S(1)}, u32[]{:S(2)}, u32[]{:S(2)}) %collective-permute-start.17) | collective-permute-done | bytes 65568 | tf_op jit(solution)/shard_map/ppermute | solution.py:22
  56.3 0.8 collective-permute-start.18
  57.0 3.6 %collective-permute-done.18 = f32[128,128]{0,1:T(8,128)S(1)} collective-permute-done((f32[128,128]{0,1:T(8,128)S(1)}, f32[128,128]{0,1:T(8,128)S(1)}, u32[]{:S(2)}, u32[]{:S(2)}) %collective-permute-start.18) | collective-permute-done | bytes 65568 | tf_op jit(solution)/shard_map/ppermute | solution.py:22
  60.6 0.8 collective-permute-start.19
  61.4 5.1 %collective-permute-done.19 = f32[128,128]{0,1:T(8,128)S(1)} collective-permute-done((f32[128,128]{0,1:T(8,128)S(1)}, f32[128,128]{0,1:T(8,128)S(1)}, u32[]{:S(2)}, u32[]{:S(2)}) %collective-permute-start.19) | collective-permute-done | bytes 65568 | tf_op jit(solution)/shard_map/ppermute | solution.py:22
  66.7 11.7 %cholesky.16 = f32[128,128]{1,0:T(8,128)S(1)} custom-call(f32[128,128]{1,0:T(8,128)S(1)} %fusion.25), custom_call_target="Cholesky" | custom-call | tf_op jit(solution)/shard_map/jit(cholesky)/cholesky | solution.py:105
  78.4 0.6 compare_reduce_fusion
  79.1 0.7 fusion.23
  79.8 9.8 %custom-call.7 = f32[1,128,128]{1,2,0:T(8,128)S(1)} custom-call(f32[1,128,128]{2,1,0:T(8,128)S(1)} %fusion.23), custom_call_target="InvertDiagBlocksLowerTriangular" | custom-call | tf_op jit(solution)/shard_map/jit(_solve_triangular)/triangular_solve | solution.py:106
  90.0 2.5 %fusion.6 = f32[256,2048]{1,0:T(8,128)S(1)} fusion(bf16[512,4096]{1,0:T(8,128)(2,1)} %param.2, bf16[512,128]{0,1:T(8,128)(2,1)S(1)} %get-tuple-element.23, bf16[512,128]{0,1:T(8,128)(2,1)S(1)} %get-tuple-element.22), kind=kOutput, calls=%fused_computation.6 | convolution fusion | flops 537395200 | bytes 4456448 | tf_op jit(solution)/shard_map/dot_general | solution.py:114
  92.8 0.7 fusion
  93.7 1.6 %collective-permute-start.20 = (bf16[4,16,2048]{2,1,0:T(8,128)(2,1)S(1)}, bf16[4,16,2048]{2,1,0:T(8,128)(2,1)S(1)}, u32[]{:S(2)}, u32[]{:S(2)}) collective-permute-start(bf16[4,16,2048]{2,1,0:T(8,128)(2,1)S(1)} %fusion.20), channel_id=1, source_target_pairs={{0,2},{2,0},{4,6},{6,4},{8,10},{10,8},{12,14},{14,12},{1,3},{3,1},... | collective-permute-start | bytes 786440 | tf_op jit(solution)/shard_map/ppermute | solution.py:22
  95.4 0.8 copy.20
  96.2 0.6 collective-permute-start.24
  96.8 4.6 %collective-permute-done.20 = bf16[4,16,2048]{2,1,0:T(8,128)(2,1)S(1)} collective-permute-done((bf16[4,16,2048]{2,1,0:T(8,128)(2,1)S(1)}, bf16[4,16,2048]{2,1,0:T(8,128)(2,1)S(1)}, u32[]{:S(2)}, u32[]{:S(2)}) %collective-permute-start.20) | collective-permute-done | bytes 262176 | tf_op jit(solution)/shard_map/ppermute | solution.py:22
  101.7 1.8 %collective-permute-start.23 = (bf16[1,16,2048]{2,1,0:T(8,128)(2,1)S(1)}, bf16[1,16,2048]{2,1,0:T(8,128)(2,1)S(1)}, u32[]{:S(2)}, u32[]{:S(2)}) collective-permute-start(bf16[1,16,2048]{2,1,0:T(8,128)(2,1)S(1)} %get-tuple-element.7), channel_id=1, source_target_pairs={{0,12},{2,14},{4,8},{6,10},{8,4},{10,6},{12,0},{14,2},{1,13},{3,15... | collective-permute-start | bytes 196616 | tf_op jit(solution)/shard_map/ppermute | solution.py:22
  103.5 1.7 %collective-permute-start.22 = (bf16[1,16,2048]{2,1,0:T(8,128)(2,1)S(1)}, bf16[1,16,2048]{2,1,0:T(8,128)(2,1)S(1)}, u32[]{:S(2)}, u32[]{:S(2)}) collective-permute-start(bf16[1,16,2048]{2,1,0:T(8,128)(2,1)S(1)} %get-tuple-element.8), channel_id=1, source_target_pairs={{0,8},{2,10},{4,12},{6,14},{8,0},{10,2},{12,4},{14,6},{1,9},{3,11}... | collective-permute-start | bytes 196616 | tf_op jit(solution)/shard_map/ppermute | solution.py:22
  105.2 1.0 collective-permute-start.25
  106.3 1.8 %collective-permute-start.27 = (bf16[1,16,2048]{2,1,0:T(8,128)(2,1)S(1)}, bf16[1,16,2048]{2,1,0:T(8,128)(2,1)S(1)}, u32[]{:S(2)}, u32[]{:S(2)}) collective-permute-start(bf16[1,16,2048]{2,1,0:T(8,128)(2,1)S(1)} %get-tuple-element.10), channel_id=1, source_target_pairs={{0,12},{2,14},{4,8},{6,10},{8,4},{10,6},{12,0},{14,2},{1,13},{3,15... | collective-permute-start | bytes 196616 | tf_op jit(solution)/shard_map/ppermute | solution.py:22
  108.0 0.8 collective-permute-start.26
  108.8 1.2 %collective-permute-done.22 = bf16[1,16,2048]{2,1,0:T(8,128)(2,1)S(1)} collective-permute-done((bf16[1,16,2048]{2,1,0:T(8,128)(2,1)S(1)}, bf16[1,16,2048]{2,1,0:T(8,128)(2,1)S(1)}, u32[]{:S(2)}, u32[]{:S(2)}) %collective-permute-start.22) | collective-permute-done | bytes 65568 | tf_op jit(solution)/shard_map/ppermute | solution.py:22
  110.2 2.1 %collective-permute-done.27 = bf16[1,16,2048]{2,1,0:T(8,128)(2,1)S(1)} collective-permute-done((bf16[1,16,2048]{2,1,0:T(8,128)(2,1)S(1)}, bf16[1,16,2048]{2,1,0:T(8,128)(2,1)S(1)}, u32[]{:S(2)}, u32[]{:S(2)}) %collective-permute-start.27) | collective-permute-done | bytes 65568 | tf_op jit(solution)/shard_map/ppermute | solution.py:22
  112.3 1.4 %collective-permute-done.26 = bf16[1,16,2048]{2,1,0:T(8,128)(2,1)S(1)} collective-permute-done((bf16[1,16,2048]{2,1,0:T(8,128)(2,1)S(1)}, bf16[1,16,2048]{2,1,0:T(8,128)(2,1)S(1)}, u32[]{:S(2)}, u32[]{:S(2)}) %collective-permute-start.26) | collective-permute-done | bytes 65568 | tf_op jit(solution)/shard_map/ppermute | solution.py:22
  113.8 0.7 pad_maximum_fusion.3
  (61 shorter events, 3.8 us)
Async XLA Ops:
  0.6 0.9 copy-start
  3.9 10.1 %collective-permute-start.8 = (bf16[4,256,128]{2,1,0:T(8,128)(2,1)S(1)}, bf16[4,256,128]{2,1,0:T(8,128)(2,1)S(1)}, u32[]{:S(2)}, u32[]{:S(2)}) collective-permute-start(bf16[4,256,128]{2,1,0:T(8,128)(2,1)S(1)} %fusion.19), channel_id=1, source_target_pairs={{0,2},{2,0},{4,6},{6,4},{8,10},{10,8},{12,14},{14,12},{1,3},{3,1},... | collective-permute-start | bytes 786440 | tf_op jit(solution)/shard_map/ppermute | solution.py:22
  9.3 9.7 %collective-permute-start = (bf16[4,256,128]{2,1,0:T(8,128)(2,1)S(1)}, bf16[4,256,128]{2,1,0:T(8,128)(2,1)S(1)}, u32[]{:S(2)}, u32[]{:S(2)}) collective-permute-start(bf16[4,256,128]{2,1,0:T(8,128)(2,1)S(1)} %fusion.18), channel_id=1, source_target_pairs={{0,2},{2,0},{4,6},{6,4},{8,10},{10,8},{12,14},{14,12},{1,3},{3,1},... | collective-permute-start | bytes 786440 | tf_op jit(solution)/shard_map/ppermute | solution.py:22
  14.2 9.2 %collective-permute-start.9 = (bf16[1,256,128]{2,1,0:T(8,128)(2,1)S(1)}, bf16[1,256,128]{2,1,0:T(8,128)(2,1)S(1)}, u32[]{:S(2)}, u32[]{:S(2)}) collective-permute-start(bf16[1,256,128]{2,1,0:T(8,128)(2,1)S(1)} %get-tuple-element.19), channel_id=1, source_target_pairs={{0,4},{2,6},{4,0},{6,2},{8,12},{10,14},{12,8},{14,10},{1,5},{3,7},... | collective-permute-start | bytes 196616 | tf_op jit(solution)/shard_map/ppermute | solution.py:22
  16.4 7.1 %collective-permute-start.11 = (bf16[1,256,128]{2,1,0:T(8,128)(2,1)S(1)}, bf16[1,256,128]{2,1,0:T(8,128)(2,1)S(1)}, u32[]{:S(2)}, u32[]{:S(2)}) collective-permute-start(bf16[1,256,128]{2,1,0:T(8,128)(2,1)S(1)} %get-tuple-element.20), channel_id=1, source_target_pairs={{0,12},{2,14},{4,8},{6,10},{8,4},{10,6},{12,0},{14,2},{1,13},{3,15... | collective-permute-start | bytes 196616 | tf_op jit(solution)/shard_map/ppermute | solution.py:22
  18.8 8.4 %collective-permute-start.10 = (bf16[1,256,128]{2,1,0:T(8,128)(2,1)S(1)}, bf16[1,256,128]{2,1,0:T(8,128)(2,1)S(1)}, u32[]{:S(2)}, u32[]{:S(2)}) collective-permute-start(bf16[1,256,128]{2,1,0:T(8,128)(2,1)S(1)} %get-tuple-element.21), channel_id=1, source_target_pairs={{0,8},{2,10},{4,12},{6,14},{8,0},{10,2},{12,4},{14,6},{1,9},{3,11}... | collective-permute-start | bytes 196616 | tf_op jit(solution)/shard_map/ppermute | solution.py:22
  19.1 8.7 %collective-permute-start.1 = (bf16[1,256,128]{2,1,0:T(8,128)(2,1)S(1)}, bf16[1,256,128]{2,1,0:T(8,128)(2,1)S(1)}, u32[]{:S(2)}, u32[]{:S(2)}) collective-permute-start(bf16[1,256,128]{2,1,0:T(8,128)(2,1)S(1)} %get-tuple-element.14), channel_id=1, source_target_pairs={{0,4},{2,6},{4,0},{6,2},{8,12},{10,14},{12,8},{14,10},{1,5},{3,7},... | collective-permute-start | bytes 196616 | tf_op jit(solution)/shard_map/ppermute | solution.py:22
  20.9 10.8 %collective-permute-start.3 = (bf16[1,256,128]{2,1,0:T(8,128)(2,1)S(1)}, bf16[1,256,128]{2,1,0:T(8,128)(2,1)S(1)}, u32[]{:S(2)}, u32[]{:S(2)}) collective-permute-start(bf16[1,256,128]{2,1,0:T(8,128)(2,1)S(1)} %get-tuple-element.15), channel_id=1, source_target_pairs={{0,12},{2,14},{4,8},{6,10},{8,4},{10,6},{12,0},{14,2},{1,13},{3,15... | collective-permute-start | bytes 196616 | tf_op jit(solution)/shard_map/ppermute | solution.py:22
  23.4 8.9 %collective-permute-start.2 = (bf16[1,256,128]{2,1,0:T(8,128)(2,1)S(1)}, bf16[1,256,128]{2,1,0:T(8,128)(2,1)S(1)}, u32[]{:S(2)}, u32[]{:S(2)}) collective-permute-start(bf16[1,256,128]{2,1,0:T(8,128)(2,1)S(1)} %get-tuple-element.16), channel_id=1, source_target_pairs={{0,8},{2,10},{4,12},{6,14},{8,0},{10,2},{12,4},{14,6},{1,9},{3,11}... | collective-permute-start | bytes 196616 | tf_op jit(solution)/shard_map/ppermute | solution.py:22
  27.3 8.2 %collective-permute-start.14 = (bf16[1,256,128]{2,1,0:T(8,128)(2,1)S(1)}, bf16[1,256,128]{2,1,0:T(8,128)(2,1)S(1)}, u32[]{:S(2)}, u32[]{:S(2)}) collective-permute-start(bf16[1,256,128]{2,1,0:T(8,128)(2,1)S(1)} %multiply_convert_fusion), channel_id=1, source_target_pairs={{0,4},{2,6},{4,0},{6,2},{8,12},{10,14},{12,8},{14,10},{1,5},{3,7},... | collective-permute-start | bytes 196616 | tf_op jit(solution)/shard_map/ppermute | solution.py:22
  27.4 9.5 %collective-permute-start.13 = (bf16[1,256,128]{2,1,0:T(8,128)(2,1)S(1)}, bf16[1,256,128]{2,1,0:T(8,128)(2,1)S(1)}, u32[]{:S(2)}, u32[]{:S(2)}) collective-permute-start(bf16[1,256,128]{2,1,0:T(8,128)(2,1)S(1)} %multiply_convert_fusion), channel_id=1, source_target_pairs={{0,8},{2,10},{4,12},{6,14},{8,0},{10,2},{12,4},{14,6},{1,9},{3,11}... | collective-permute-start | bytes 196616 | tf_op jit(solution)/shard_map/ppermute | solution.py:22
  27.8 9.1 %collective-permute-start.12 = (bf16[1,256,128]{2,1,0:T(8,128)(2,1)S(1)}, bf16[1,256,128]{2,1,0:T(8,128)(2,1)S(1)}, u32[]{:S(2)}, u32[]{:S(2)}) collective-permute-start(bf16[1,256,128]{2,1,0:T(8,128)(2,1)S(1)} %multiply_convert_fusion), channel_id=1, source_target_pairs={{0,12},{2,14},{4,8},{6,10},{8,4},{10,6},{12,0},{14,2},{1,13},{3,15... | collective-permute-start | bytes 196616 | tf_op jit(solution)/shard_map/ppermute | solution.py:22
  32.4 6.1 %collective-permute-start.6 = (bf16[1,256,128]{2,1,0:T(8,128)(2,1)S(1)}, bf16[1,256,128]{2,1,0:T(8,128)(2,1)S(1)}, u32[]{:S(2)}, u32[]{:S(2)}) collective-permute-start(bf16[1,256,128]{2,1,0:T(8,128)(2,1)S(1)} %multiply_convert_fusion.1), channel_id=1, source_target_pairs={{0,4},{2,6},{4,0},{6,2},{8,12},{10,14},{12,8},{14,10},{1,5},{3,7},... | collective-permute-start | bytes 196616 | tf_op jit(solution)/shard_map/ppermute | solution.py:22
  32.5 7.3 %collective-permute-start.5 = (bf16[1,256,128]{2,1,0:T(8,128)(2,1)S(1)}, bf16[1,256,128]{2,1,0:T(8,128)(2,1)S(1)}, u32[]{:S(2)}, u32[]{:S(2)}) collective-permute-start(bf16[1,256,128]{2,1,0:T(8,128)(2,1)S(1)} %multiply_convert_fusion.1), channel_id=1, source_target_pairs={{0,8},{2,10},{4,12},{6,14},{8,0},{10,2},{12,4},{14,6},{1,9},{3,11}... | collective-permute-start | bytes 196616 | tf_op jit(solution)/shard_map/ppermute | solution.py:22
  35.5 6.1 %collective-permute-start.4 = (bf16[1,256,128]{2,1,0:T(8,128)(2,1)S(1)}, bf16[1,256,128]{2,1,0:T(8,128)(2,1)S(1)}, u32[]{:S(2)}, u32[]{:S(2)}) collective-permute-start(bf16[1,256,128]{2,1,0:T(8,128)(2,1)S(1)} %multiply_convert_fusion.1), channel_id=1, source_target_pairs={{0,12},{2,14},{4,8},{6,10},{8,4},{10,6},{12,0},{14,2},{1,13},{3,15... | collective-permute-start | bytes 196616 | tf_op jit(solution)/shard_map/ppermute | solution.py:22
  36.9 9.1 %copy-start.1 = (bf16[512,4096]{1,0:T(8,128)(2,1)S(1)}, bf16[512,4096]{1,0:T(8,128)(2,1)}, u32[]{:S(2)}) copy-start(bf16[512,4096]{1,0:T(8,128)(2,1)} %param.2) | copy-start | bytes 12582916
  36.9 8.9 %collective-permute-start.15 = (bf16[4,256,128]{2,1,0:T(8,128)(2,1)S(1)}, bf16[4,256,128]{2,1,0:T(8,128)(2,1)S(1)}, u32[]{:S(2)}, u32[]{:S(2)}) collective-permute-start(bf16[4,256,128]{2,1,0:T(8,128)(2,1)S(1)} %maximum_bitcast_fusion.1), channel_id=1, source_target_pairs={{0,2},{2,0},{4,6},{6,4},{8,10},{10,8},{12,14},{14,12},{1,3},{3,1},... | collective-permute-start | bytes 786440 | tf_op jit(solution)/shard_map/ppermute | solution.py:22
  41.6 7.4 %collective-permute-start.7 = (bf16[4,256,128]{2,1,0:T(8,128)(2,1)S(1)}, bf16[4,256,128]{2,1,0:T(8,128)(2,1)S(1)}, u32[]{:S(2)}, u32[]{:S(2)}) collective-permute-start(bf16[4,256,128]{2,1,0:T(8,128)(2,1)S(1)} %maximum_bitcast_fusion), channel_id=1, source_target_pairs={{0,2},{2,0},{4,6},{6,4},{8,10},{10,8},{12,14},{14,12},{1,3},{3,1},... | collective-permute-start | bytes 786440 | tf_op jit(solution)/shard_map/ppermute | solution.py:22
  49.9 1.6 %collective-permute-start.16 = (f32[512,128]{0,1:T(8,128)S(1)}, f32[512,128]{0,1:T(8,128)S(1)}, u32[]{:S(2)}, u32[]{:S(2)}) collective-permute-start(f32[512,128]{0,1:T(8,128)S(1)} %fusion.15), channel_id=1, source_target_pairs={{0,1},{1,0},{2,3},{3,2},{4,5},{5,4},{6,7},{7,6},{8,9},{9,8},{10,11... | collective-permute-start | bytes 786440 | tf_op jit(solution)/shard_map/ppermute | solution.py:22
  51.9 4.3 %collective-permute-start.17 = (f32[128,128]{0,1:T(8,128)S(1)}, f32[128,128]{0,1:T(8,128)S(1)}, u32[]{:S(2)}, u32[]{:S(2)}) collective-permute-start(f32[128,128]{0,1:T(8,128)S(1)} %fusion.22), channel_id=1, source_target_pairs={{0,2},{2,0},{4,6},{6,4},{8,10},{10,8},{12,14},{14,12},{1,3},{3,1},... | collective-permute-start | bytes 196616 | tf_op jit(solution)/shard_map/ppermute | solution.py:22
  56.3 4.3 %collective-permute-start.18 = (f32[128,128]{0,1:T(8,128)S(1)}, f32[128,128]{0,1:T(8,128)S(1)}, u32[]{:S(2)}, u32[]{:S(2)}) collective-permute-start(f32[128,128]{0,1:T(8,128)S(1)} %add.141), channel_id=1, source_target_pairs={{0,4},{2,6},{4,0},{6,2},{8,12},{10,14},{12,8},{14,10},{1,5},{3,7},... | collective-permute-start | bytes 196616 | tf_op jit(solution)/shard_map/ppermute | solution.py:22
  60.6 5.9 %collective-permute-start.19 = (f32[128,128]{0,1:T(8,128)S(1)}, f32[128,128]{0,1:T(8,128)S(1)}, u32[]{:S(2)}, u32[]{:S(2)}) collective-permute-start(f32[128,128]{0,1:T(8,128)S(1)} %add.142), channel_id=1, source_target_pairs={{0,8},{2,10},{4,12},{6,14},{8,0},{10,2},{12,4},{14,6},{1,9},{3,11}... | collective-permute-start | bytes 196616 | tf_op jit(solution)/shard_map/ppermute | solution.py:22
  90.0 2.8 %copy-start.2 = (bf16[512,4096]{1,0:T(8,128)(2,1)S(1)}, bf16[512,4096]{1,0:T(8,128)(2,1)}, u32[]{:S(2)}) copy-start(bf16[512,4096]{1,0:T(8,128)(2,1)} %param.2) | copy-start | bytes 12582916
  93.7 7.8 %collective-permute-start.20 = (bf16[4,16,2048]{2,1,0:T(8,128)(2,1)S(1)}, bf16[4,16,2048]{2,1,0:T(8,128)(2,1)S(1)}, u32[]{:S(2)}, u32[]{:S(2)}) collective-permute-start(bf16[4,16,2048]{2,1,0:T(8,128)(2,1)S(1)} %fusion.20), channel_id=1, source_target_pairs={{0,2},{2,0},{4,6},{6,4},{8,10},{10,8},{12,14},{14,12},{1,3},{3,1},... | collective-permute-start | bytes 786440 | tf_op jit(solution)/shard_map/ppermute | solution.py:22
  96.2 8.9 %collective-permute-start.24 = (bf16[4,16,2048]{2,1,0:T(8,128)(2,1)S(1)}, bf16[4,16,2048]{2,1,0:T(8,128)(2,1)S(1)}, u32[]{:S(2)}, u32[]{:S(2)}) collective-permute-start(bf16[4,16,2048]{2,1,0:T(8,128)(2,1)S(1)} %fusion.21), channel_id=1, source_target_pairs={{0,2},{2,0},{4,6},{6,4},{8,10},{10,8},{12,14},{14,12},{1,3},{3,1},... | collective-permute-start | bytes 786440 | tf_op jit(solution)/shard_map/ppermute | solution.py:22
  101.6 6.5 %collective-permute-start.21 = (bf16[1,16,2048]{2,1,0:T(8,128)(2,1)S(1)}, bf16[1,16,2048]{2,1,0:T(8,128)(2,1)S(1)}, u32[]{:S(2)}, u32[]{:S(2)}) collective-permute-start(bf16[1,16,2048]{2,1,0:T(8,128)(2,1)S(1)} %get-tuple-element.6), channel_id=1, source_target_pairs={{0,4},{2,6},{4,0},{6,2},{8,12},{10,14},{12,8},{14,10},{1,5},{3,7},... | collective-permute-start | bytes 196616 | tf_op jit(solution)/shard_map/ppermute | solution.py:22
  101.7 7.1 %collective-permute-start.23 = (bf16[1,16,2048]{2,1,0:T(8,128)(2,1)S(1)}, bf16[1,16,2048]{2,1,0:T(8,128)(2,1)S(1)}, u32[]{:S(2)}, u32[]{:S(2)}) collective-permute-start(bf16[1,16,2048]{2,1,0:T(8,128)(2,1)S(1)} %get-tuple-element.7), channel_id=1, source_target_pairs={{0,12},{2,14},{4,8},{6,10},{8,4},{10,6},{12,0},{14,2},{1,13},{3,15... | collective-permute-start | bytes 196616 | tf_op jit(solution)/shard_map/ppermute | solution.py:22
  103.5 6.5 %collective-permute-start.22 = (bf16[1,16,2048]{2,1,0:T(8,128)(2,1)S(1)}, bf16[1,16,2048]{2,1,0:T(8,128)(2,1)S(1)}, u32[]{:S(2)}, u32[]{:S(2)}) collective-permute-start(bf16[1,16,2048]{2,1,0:T(8,128)(2,1)S(1)} %get-tuple-element.8), channel_id=1, source_target_pairs={{0,8},{2,10},{4,12},{6,14},{8,0},{10,2},{12,4},{14,6},{1,9},{3,11}... | collective-permute-start | bytes 196616 | tf_op jit(solution)/shard_map/ppermute | solution.py:22
  105.2 5.0 %collective-permute-start.25 = (bf16[1,16,2048]{2,1,0:T(8,128)(2,1)S(1)}, bf16[1,16,2048]{2,1,0:T(8,128)(2,1)S(1)}, u32[]{:S(2)}, u32[]{:S(2)}) collective-permute-start(bf16[1,16,2048]{2,1,0:T(8,128)(2,1)S(1)} %get-tuple-element.9), channel_id=1, source_target_pairs={{0,4},{2,6},{4,0},{6,2},{8,12},{10,14},{12,8},{14,10},{1,5},{3,7},... | collective-permute-start | bytes 196616 | tf_op jit(solution)/shard_map/ppermute | solution.py:22
  106.3 6.1 %collective-permute-start.27 = (bf16[1,16,2048]{2,1,0:T(8,128)(2,1)S(1)}, bf16[1,16,2048]{2,1,0:T(8,128)(2,1)S(1)}, u32[]{:S(2)}, u32[]{:S(2)}) collective-permute-start(bf16[1,16,2048]{2,1,0:T(8,128)(2,1)S(1)} %get-tuple-element.10), channel_id=1, source_target_pairs={{0,12},{2,14},{4,8},{6,10},{8,4},{10,6},{12,0},{14,2},{1,13},{3,15... | collective-permute-start | bytes 196616 | tf_op jit(solution)/shard_map/ppermute | solution.py:22
  108.0 5.7 %collective-permute-start.26 = (bf16[1,16,2048]{2,1,0:T(8,128)(2,1)S(1)}, bf16[1,16,2048]{2,1,0:T(8,128)(2,1)S(1)}, u32[]{:S(2)}, u32[]{:S(2)}) collective-permute-start(bf16[1,16,2048]{2,1,0:T(8,128)(2,1)S(1)} %get-tuple-element.11), channel_id=1, source_target_pairs={{0,8},{2,10},{4,12},{6,14},{8,0},{10,2},{12,4},{14,6},{1,9},{3,11}... | collective-permute-start | bytes 196616 | tf_op jit(solution)/shard_map/ppermute | solution.py:22

commit v3 on v2

--- a/solution.py
+++ b/solution.py
@@ -1,8 +1,11 @@
+import functools
 import math
 
 import jax
 import jax.numpy as jnp
 from jax import lax
+from jax.experimental import pallas as pl
+from jax.experimental.pallas import tpu as pltpu
 from jax.sharding import PartitionSpec as P
 
 CHUNKS = 2
@@ -70,6 +73,108 @@
     return blocks
 
 
+def matmul(left, right, exact=True):
+    if not exact:
+        left, right = left.astype(jnp.bfloat16), right.astype(jnp.bfloat16)
+    return lax.dot_general(
+        left,
+        right,
+        (((1,), (0,)), ((), ())),
+        precision=lax.Precision.HIGHEST if exact else None,
+        preferred_element_type=jnp.float32,
+    )
+
+
+def matmul_t(left, right, exact=True):
+    if not exact:
+        left, right = left.astype(jnp.bfloat16), right.astype(jnp.bfloat16)
+    return lax.dot_general(
+        left,
+        right,
+        (((1,), (1,)), ((), ())),
+        precision=lax.Precision.HIGHEST if exact else None,
+        preferred_element_type=jnp.float32,
+    )
+
+
+UPDATES = 4
+LOOSE_UPDATES = 2
+CLOSE = 1e-5
+
+
+def basis_kernel(total_cols, root_rows, gram_ref, mine_ref, other_ref, *refs):
+    basis_ref, pair_ref, work_ref, inverse_ref = refs
+    width = gram_ref.shape[0]
+    row = lax.broadcasted_iota(jnp.int32, (width, width), 0)
+    col = lax.broadcasted_iota(jnp.int32, (width, width), 1)
+    on_diag = row == col
+    unit = jnp.where(on_diag, 1.0, 0.0)
+    half = jnp.where(row > col, 1.0, jnp.where(on_diag, 0.5, 0.0))
+
+    gram = gram_ref[...]
+    diagonal = jnp.where(on_diag, gram, 0.0)
+    down = lax.rsqrt(jnp.sum(diagonal, axis=1, keepdims=True))
+    across = lax.rsqrt(jnp.sum(diagonal, axis=0, keepdims=True))
+    scaled = gram * down * across
+
+    error = scaled - unit
+    step = error * half
+    inverse = unit - step + matmul(step, step, False)
+    for update in range(1, UPDATES):
+        exact = update >= LOOSE_UPDATES
+        error = matmul_t(matmul(inverse, scaled, exact), inverse, exact) - unit
+        step = error * half
+        inverse = inverse - matmul(step, inverse - matmul(step, inverse, exact), exact)
+    inverse_ref[...] = inverse * across
+    far = jnp.sum(error * error)
+
+    @pl.when(jnp.logical_not(far <= CLOSE))
+    def _():
+        work_ref[...] = gram
+        inverse_ref[...] = unit
+
+        def eliminate(k, carry):
+            whole = work_ref[...]
+            pivot_row = work_ref[pl.ds(k, 1), :]
+            pivot = jnp.sum(
+                jnp.where(col[:1] == k, pivot_row, 0.0), axis=1, keepdims=True
+            )
+            column = jnp.sum(jnp.where(col == k, whole, 0.0), axis=1, keepdims=True)
+            factor = jnp.where(row[:, :1] > k, column / pivot, 0.0)
+            work_ref[...] = whole - factor * pivot_row
+            inverse_ref[...] = inverse_ref[...] - factor * inverse_ref[pl.ds(k, 1), :]
+            return carry
+
+        lax.fori_loop(0, width, eliminate, 0)
+        pivots = jnp.sum(jnp.where(on_diag, work_ref[...], 0.0), axis=1, keepdims=True)
+        inverse_ref[...] = inverse_ref[...] * lax.rsqrt(pivots)
+
+    sketch = (mine_ref[...] + other_ref[...]) / total_cols
+    basis = matmul_t(sketch, inverse_ref[...]) * root_rows
+    basis_ref[...] = basis
+    high = basis.astype(jnp.bfloat16)
+    pair_ref[:, :width] = high
+    pair_ref[:, width:] = (basis - high.astype(jnp.float32)).astype(jnp.bfloat16)
+
+
+def make_basis(gram, mine, other, total_cols, root_rows):
+    rows, width = mine.shape
+    return pl.pallas_call(
+        functools.partial(basis_kernel, total_cols, root_rows),
+        out_shape=(
+            jax.ShapeDtypeStruct((rows, width), jnp.float32),
+            jax.ShapeDtypeStruct((rows, 2 * width), jnp.bfloat16),
+        ),
+        in_specs=[pl.BlockSpec(memory_space=pltpu.VMEM)] * 3,
+        out_specs=[pl.BlockSpec(memory_space=pltpu.VMEM)] * 2,
+        scratch_shapes=[
+            pltpu.VMEM((width, width), jnp.float32),
+            pltpu.VMEM((width, width), jnp.float32),
+        ],
+        name="make_basis",
+    )(gram, mine, other)
+
+
 def per_device(activations, start_sketch):
     rows_here, cols_here = activations.shape
     width = start_sketch.shape[1]
@@ -96,19 +201,15 @@
             chunk.reshape(cols_chunk, width),
             preferred_element_type=jnp.float32,
         )
-    sketch = exchange_sum(partial_sketch, "col") / total_cols
+    other_sketch = swap(partial_sketch, "col", 1)
+    sketch = (partial_sketch + other_sketch) / total_cols
 
     local_gram = lax.dot_general(
         sketch, sketch, (((0,), (0,)), ((), ())), precision=lax.Precision.HIGHEST
     )
     gram = exchange_sum(local_gram, "row")
-    factor = jnp.linalg.cholesky(gram)
-    solved = jax.scipy.linalg.solve_triangular(factor, sketch.T, lower=True)
-    basis = solved.T * root_rows
-
-    high = basis.astype(jnp.bfloat16)
-    low = (basis - high.astype(jnp.float32)).astype(jnp.bfloat16)
-    pair = jnp.concatenate([high, low], axis=1)
+    basis, pair = make_basis(gram, partial_sketch, other_sketch, total_cols, root_rows)
+
     pieces = []
     for span in spans:
         local_pair = lax.dot_general(

time: 115 us -> 97 us (0.84)
  other arithmetic: 24.5 us -> 2.32 us
  Pallas kernels: 0 us -> 4.8 us
    another operation x5 -> x0, other arithmetic: 22.9 us -> none  [the longest x3 12.4 us: per_device(): factor = jnp.linalg.cholesky(gram)]
    pallas_call x0 -> x1, Pallas kernels: none -> 4.8 us  [make_basis(): pl.pallas_call(functools.partial(basis_kernel, total_cols, root_rows), ou...]
where the time goes in v3:
time: 97 us; the launch traced here: 96.8 us
  waiting for transfers between devices  40.4 us (42%)
  starting transfers between devices  36.7 us (38%)
  matrix products  9.95 us (10%)
  Pallas kernels  4.8 us (5%)
  other arithmetic  2.32 us (2%)
  local copies, waits for them, and re-layouts  1.62 us (2%)
    ppermute x28, waiting for transfers between devices, swap(): return lax.ppermute(value, axis, [(i, i ^ distance) for i in range(size)])  40.4 us
    ppermute x28, starting transfers between devices, swap(): return lax.ppermute(value, axis, [(i, i ^ distance) for i in range(size)])  36.7 us
    pallas_call x1, Pallas kernels, make_basis(): pl.pallas_call(functools.partial(basis_kernel, total_cols, root_rows), ou...  4.8 us
    dot_general x2, matrix products, per_device(): lax.dot_general(activations[:, span], start_sketch, (((0,), (0,)), ((), (...  4.65 us
    dot_general x2, matrix products, per_device(): lax.dot_general(pair, activations[:, span], (((0,), (0,)), ((), ())), pre...  3.27 us
  transfers between devices with their start and end apart: 28, of which 16 were waited for; matrix products, arithmetic and copies ran while one was open for 4% of the time, Pallas kernels for 0%

profile of v3, /device:TPU:0, one launch (start us, length us, event | category | flops | bytes accessed | tf_op | source)
XLA Modules:
  0.0 96.8 jit_solution(16189816325639212911)
XLA Ops:
  0.7 0.9 copy-done
  1.5 2.3 %fusion.4 = f32[2048,128]{1,0:T(8,128)S(1)} fusion(bf16[512,128]{1,0:T(8,128)(2,1)S(1)} %copy-done, bf16[512,4096]{1,0:T(8,128)(2,1)} %param.2), kind=kOutput, calls=%fused_computation.4 | convolution fusion | flops 268435456 | bytes 3276800 | tf_op jit(solution)/shard_map/dot_general | solution.py:191
  3.9 3.0 %collective-permute-start.8 = (bf16[4,256,128]{2,1,0:T(8,128)(2,1)S(1)}, bf16[4,256,128]{2,1,0:T(8,128)(2,1)S(1)}, u32[]{:S(2)}, u32[]{:S(2)}) collective-permute-start(bf16[4,256,128]{2,1,0:T(8,128)(2,1)S(1)} %fusion.19), channel_id=1, source_target_pairs={{0,2},{2,0},{4,6},{6,4},{8,10},{10,8},{12,14},{14,12},{1,3},{3,1},... | collective-permute-start | bytes 786440 | tf_op jit(solution)/shard_map/ppermute | solution.py:25
  6.9 2.3 %fusion.10 = f32[2048,128]{1,0:T(8,128)S(1)} fusion(bf16[512,128]{1,0:T(8,128)(2,1)S(1)} %copy-done, bf16[512,4096]{1,0:T(8,128)(2,1)} %param.2), kind=kOutput, calls=%fused_computation.10 | convolution fusion | flops 268435456 | bytes 3276800 | tf_op jit(solution)/shard_map/dot_general | solution.py:191
  9.4 4.6 %collective-permute-done.8 = bf16[4,256,128]{2,1,0:T(8,128)(2,1)S(1)} collective-permute-done((bf16[4,256,128]{2,1,0:T(8,128)(2,1)S(1)}, bf16[4,256,128]{2,1,0:T(8,128)(2,1)S(1)}, u32[]{:S(2)}, u32[]{:S(2)}) %collective-permute-start.8) | collective-permute-done | bytes 262176 | tf_op jit(solution)/shard_map/ppermute | solution.py:25
  14.2 2.2 %collective-permute-start.9 = (bf16[1,256,128]{2,1,0:T(8,128)(2,1)S(1)}, bf16[1,256,128]{2,1,0:T(8,128)(2,1)S(1)}, u32[]{:S(2)}, u32[]{:S(2)}) collective-permute-start(bf16[1,256,128]{2,1,0:T(8,128)(2,1)S(1)} %get-tuple-element.19), channel_id=1, source_target_pairs={{0,4},{2,6},{4,0},{6,2},{8,12},{10,14},{12,8},{14,10},{1,5},{3,7},... | collective-permute-start | bytes 196616 | tf_op jit(solution)/shard_map/ppermute | solution.py:25
  16.4 2.5 %collective-permute-start.11 = (bf16[1,256,128]{2,1,0:T(8,128)(2,1)S(1)}, bf16[1,256,128]{2,1,0:T(8,128)(2,1)S(1)}, u32[]{:S(2)}, u32[]{:S(2)}) collective-permute-start(bf16[1,256,128]{2,1,0:T(8,128)(2,1)S(1)} %get-tuple-element.20), channel_id=1, source_target_pairs={{0,12},{2,14},{4,8},{6,10},{8,4},{10,6},{12,0},{14,2},{1,13},{3,15... | collective-permute-start | bytes 196616 | tf_op jit(solution)/shard_map/ppermute | solution.py:25
  19.1 1.9 %collective-permute-start.1 = (bf16[1,256,128]{2,1,0:T(8,128)(2,1)S(1)}, bf16[1,256,128]{2,1,0:T(8,128)(2,1)S(1)}, u32[]{:S(2)}, u32[]{:S(2)}) collective-permute-start(bf16[1,256,128]{2,1,0:T(8,128)(2,1)S(1)} %get-tuple-element.14), channel_id=1, source_target_pairs={{0,4},{2,6},{4,0},{6,2},{8,12},{10,14},{12,8},{14,10},{1,5},{3,7},... | collective-permute-start | bytes 196616 | tf_op jit(solution)/shard_map/ppermute | solution.py:25
  20.9 2.5 %collective-permute-start.3 = (bf16[1,256,128]{2,1,0:T(8,128)(2,1)S(1)}, bf16[1,256,128]{2,1,0:T(8,128)(2,1)S(1)}, u32[]{:S(2)}, u32[]{:S(2)}) collective-permute-start(bf16[1,256,128]{2,1,0:T(8,128)(2,1)S(1)} %get-tuple-element.15), channel_id=1, source_target_pairs={{0,12},{2,14},{4,8},{6,10},{8,4},{10,6},{12,0},{14,2},{1,13},{3,15... | collective-permute-start | bytes 196616 | tf_op jit(solution)/shard_map/ppermute | solution.py:25
  23.4 3.8 %collective-permute-done.10 = bf16[1,256,128]{2,1,0:T(8,128)(2,1)S(1)} collective-permute-done((bf16[1,256,128]{2,1,0:T(8,128)(2,1)S(1)}, bf16[1,256,128]{2,1,0:T(8,128)(2,1)S(1)}, u32[]{:S(2)}, u32[]{:S(2)}) %collective-permute-start.10) | collective-permute-done | bytes 65568 | tf_op jit(solution)/shard_map/ppermute | solution.py:25
  27.4 0.4 collective-permute-start.13
  27.8 4.0 %collective-permute-start.12 = (bf16[1,256,128]{2,1,0:T(8,128)(2,1)S(1)}, bf16[1,256,128]{2,1,0:T(8,128)(2,1)S(1)}, u32[]{:S(2)}, u32[]{:S(2)}) collective-permute-start(bf16[1,256,128]{2,1,0:T(8,128)(2,1)S(1)} %multiply_convert_fusion), channel_id=1, source_target_pairs={{0,12},{2,14},{4,8},{6,10},{8,4},{10,6},{12,0},{14,2},{1,13},{3,15... | collective-permute-start | bytes 196616 | tf_op jit(solution)/shard_map/ppermute | solution.py:25
  31.8 0.6 collective-permute-done.2
  32.5 3.0 %collective-permute-start.5 = (bf16[1,256,128]{2,1,0:T(8,128)(2,1)S(1)}, bf16[1,256,128]{2,1,0:T(8,128)(2,1)S(1)}, u32[]{:S(2)}, u32[]{:S(2)}) collective-permute-start(bf16[1,256,128]{2,1,0:T(8,128)(2,1)S(1)} %multiply_convert_fusion.1), channel_id=1, source_target_pairs={{0,8},{2,10},{4,12},{6,14},{8,0},{10,2},{12,4},{14,6},{1,9},{3,11}... | collective-permute-start | bytes 196616 | tf_op jit(solution)/shard_map/ppermute | solution.py:25
  35.5 1.4 %collective-permute-start.4 = (bf16[1,256,128]{2,1,0:T(8,128)(2,1)S(1)}, bf16[1,256,128]{2,1,0:T(8,128)(2,1)S(1)}, u32[]{:S(2)}, u32[]{:S(2)}) collective-permute-start(bf16[1,256,128]{2,1,0:T(8,128)(2,1)S(1)} %multiply_convert_fusion.1), channel_id=1, source_target_pairs={{0,12},{2,14},{4,8},{6,10},{8,4},{10,6},{12,0},{14,2},{1,13},{3,15... | collective-permute-start | bytes 196616 | tf_op jit(solution)/shard_map/ppermute | solution.py:25
  36.9 1.6 %collective-permute-start.15 = (bf16[4,256,128]{2,1,0:T(8,128)(2,1)S(1)}, bf16[4,256,128]{2,1,0:T(8,128)(2,1)S(1)}, u32[]{:S(2)}, u32[]{:S(2)}) collective-permute-start(bf16[4,256,128]{2,1,0:T(8,128)(2,1)S(1)} %maximum_bitcast_fusion.1), channel_id=1, source_target_pairs={{0,2},{2,0},{4,6},{6,4},{8,10},{10,8},{12,14},{14,12},{1,3},{3,1},... | collective-permute-start | bytes 786440 | tf_op jit(solution)/shard_map/ppermute | solution.py:25
  38.5 1.3 %collective-permute-done.5 = bf16[1,256,128]{2,1,0:T(8,128)(2,1)S(1)} collective-permute-done((bf16[1,256,128]{2,1,0:T(8,128)(2,1)S(1)}, bf16[1,256,128]{2,1,0:T(8,128)(2,1)S(1)}, u32[]{:S(2)}, u32[]{:S(2)}) %collective-permute-start.5) | collective-permute-done | bytes 65568 | tf_op jit(solution)/shard_map/ppermute | solution.py:25
  39.8 1.7 %collective-permute-done.4 = bf16[1,256,128]{2,1,0:T(8,128)(2,1)S(1)} collective-permute-done((bf16[1,256,128]{2,1,0:T(8,128)(2,1)S(1)}, bf16[1,256,128]{2,1,0:T(8,128)(2,1)S(1)}, u32[]{:S(2)}, u32[]{:S(2)}) %collective-permute-start.4) | collective-permute-done | bytes 65568 | tf_op jit(solution)/shard_map/ppermute | solution.py:25
  41.6 1.6 %collective-permute-start.7 = (bf16[4,256,128]{2,1,0:T(8,128)(2,1)S(1)}, bf16[4,256,128]{2,1,0:T(8,128)(2,1)S(1)}, u32[]{:S(2)}, u32[]{:S(2)}) collective-permute-start(bf16[4,256,128]{2,1,0:T(8,128)(2,1)S(1)} %maximum_bitcast_fusion), channel_id=1, source_target_pairs={{0,2},{2,0},{4,6},{6,4},{8,10},{10,8},{12,14},{14,12},{1,3},{3,1},... | collective-permute-start | bytes 786440 | tf_op jit(solution)/shard_map/ppermute | solution.py:25
  43.2 2.6 %collective-permute-done.15 = bf16[4,256,128]{2,1,0:T(8,128)(2,1)S(1)} collective-permute-done((bf16[4,256,128]{2,1,0:T(8,128)(2,1)S(1)}, bf16[4,256,128]{2,1,0:T(8,128)(2,1)S(1)}, u32[]{:S(2)}, u32[]{:S(2)}) %collective-permute-start.15) | collective-permute-done | bytes 262176 | tf_op jit(solution)/shard_map/ppermute | solution.py:25
  46.0 0.7 fusion.2
  46.7 2.3 %collective-permute-done.7 = bf16[4,256,128]{2,1,0:T(8,128)(2,1)S(1)} collective-permute-done((bf16[4,256,128]{2,1,0:T(8,128)(2,1)S(1)}, bf16[4,256,128]{2,1,0:T(8,128)(2,1)S(1)}, u32[]{:S(2)}, u32[]{:S(2)}) %collective-permute-start.7) | collective-permute-done | bytes 262176 | tf_op jit(solution)/shard_map/ppermute | solution.py:25
  49.1 0.7 fusion.15.mine_ref
  49.9 1.5 %collective-permute-done.16.other_ref = f32[512,128]{1,0:T(8,128)S(1)} collective-permute-done((f32[512,128]{1,0:T(8,128)S(1)}, f32[512,128]{1,0:T(8,128)S(1)}, u32[]{:S(2)}, u32[]{:S(2)}) %collective-permute-start.16) | collective-permute-done | bytes 262176 | tf_op jit(solution)/shard_map/ppermute | solution.py:25
  51.4 0.6 fusion.22
  52.0 1.6 %collective-permute-start.17 = (f32[128,128]{1,0:T(8,128)S(1)}, f32[128,128]{1,0:T(8,128)S(1)}, u32[]{:S(2)}, u32[]{:S(2)}) collective-permute-start(f32[128,128]{1,0:T(8,128)S(1)} %fusion.22), channel_id=1, source_target_pairs={{0,2},{2,0},{4,6},{6,4},{8,10},{10,8},{12,14},{14,12},{1,3},{3,1},... | collective-permute-start | bytes 196616 | tf_op jit(solution)/shard_map/ppermute | solution.py:25
  53.6 2.8 %collective-permute-done.17 = f32[128,128]{1,0:T(8,128)S(1)} collective-permute-done((f32[128,128]{1,0:T(8,128)S(1)}, f32[128,128]{1,0:T(8,128)S(1)}, u32[]{:S(2)}, u32[]{:S(2)}) %collective-permute-start.17) | collective-permute-done | bytes 65568 | tf_op jit(solution)/shard_map/ppermute | solution.py:25
  56.4 0.7 collective-permute-start.18
  57.1 3.6 %collective-permute-done.18 = f32[128,128]{1,0:T(8,128)S(1)} collective-permute-done((f32[128,128]{1,0:T(8,128)S(1)}, f32[128,128]{1,0:T(8,128)S(1)}, u32[]{:S(2)}, u32[]{:S(2)}) %collective-permute-start.18) | collective-permute-done | bytes 65568 | tf_op jit(solution)/shard_map/ppermute | solution.py:25
  60.7 0.8 collective-permute-start.19
  61.5 5.1 %collective-permute-done.19 = f32[128,128]{1,0:T(8,128)S(1)} collective-permute-done((f32[128,128]{1,0:T(8,128)S(1)}, f32[128,128]{1,0:T(8,128)S(1)}, u32[]{:S(2)}, u32[]{:S(2)}) %collective-permute-start.19) | collective-permute-done | bytes 65568 | tf_op jit(solution)/shard_map/ppermute | solution.py:25
  66.7 0.6 add.130.gram_ref
  67.3 4.8 %make_basis.1 = (f32[512,128]{1,0:T(8,128)}, bf16[512,256]{1,0:T(8,128)(2,1)}) custom-call(f32[128,128]{1,0:T(8,128)} %add.130.gram_ref, f32[512,128]{1,0:T(8,128)} %copy-done.4, f32[512,128]{1,0:T(8,128)} %copy-done.5), custom_call_target="tpu_custom_call" | custom-call | tf_op jit(solution)/shard_map/make_basis/pallas_call | solution.py:162
  72.1 2.5 %fusion = f32[256,2048]{1,0:T(8,128)S(1)} fusion(bf16[512,256]{1,0:T(8,128)(2,1)} %get-tuple-element.5, bf16[512,4096]{1,0:T(8,128)(2,1)} %param.2), kind=kOutput, calls=%fused_computation | convolution fusion | flops 536870912 | bytes 4456448 | tf_op jit(solution)/shard_map/dot_general | solution.py:215
  74.7 0.3 copy-done.2
  75.0 0.7 fusion.6
  75.9 1.6 %collective-permute-start.24 = (bf16[4,16,2048]{2,1,0:T(8,128)(2,1)S(1)}, bf16[4,16,2048]{2,1,0:T(8,128)(2,1)S(1)}, u32[]{:S(2)}, u32[]{:S(2)}) collective-permute-start(bf16[4,16,2048]{2,1,0:T(8,128)(2,1)S(1)} %fusion.21), channel_id=1, source_target_pairs={{0,2},{2,0},{4,6},{6,4},{8,10},{10,8},{12,14},{14,12},{1,3},{3,1},... | collective-permute-start | bytes 786440 | tf_op jit(solution)/shard_map/ppermute | solution.py:25
  77.7 0.6 collective-permute-start.20
  78.3 5.5 %collective-permute-done.24 = bf16[4,16,2048]{2,1,0:T(8,128)(2,1)S(1)} collective-permute-done((bf16[4,16,2048]{2,1,0:T(8,128)(2,1)S(1)}, bf16[4,16,2048]{2,1,0:T(8,128)(2,1)S(1)}, u32[]{:S(2)}, u32[]{:S(2)}) %collective-permute-start.24) | collective-permute-done | bytes 262176 | tf_op jit(solution)/shard_map/ppermute | solution.py:25
  84.0 1.8 %collective-permute-start.27 = (bf16[1,16,2048]{2,1,0:T(8,128)(2,1)S(1)}, bf16[1,16,2048]{2,1,0:T(8,128)(2,1)S(1)}, u32[]{:S(2)}, u32[]{:S(2)}) collective-permute-start(bf16[1,16,2048]{2,1,0:T(8,128)(2,1)S(1)} %get-tuple-element.10), channel_id=1, source_target_pairs={{0,12},{2,14},{4,8},{6,10},{8,4},{10,6},{12,0},{14,2},{1,13},{3,15... | collective-permute-start | bytes 196616 | tf_op jit(solution)/shard_map/ppermute | solution.py:25
  85.7 1.7 %collective-permute-start.26 = (bf16[1,16,2048]{2,1,0:T(8,128)(2,1)S(1)}, bf16[1,16,2048]{2,1,0:T(8,128)(2,1)S(1)}, u32[]{:S(2)}, u32[]{:S(2)}) collective-permute-start(bf16[1,16,2048]{2,1,0:T(8,128)(2,1)S(1)} %get-tuple-element.11), channel_id=1, source_target_pairs={{0,8},{2,10},{4,12},{6,14},{8,0},{10,2},{12,4},{14,6},{1,9},{3,11}... | collective-permute-start | bytes 196616 | tf_op jit(solution)/shard_map/ppermute | solution.py:25
  87.5 1.0 %collective-permute-start.21 = (bf16[1,16,2048]{2,1,0:T(8,128)(2,1)S(1)}, bf16[1,16,2048]{2,1,0:T(8,128)(2,1)S(1)}, u32[]{:S(2)}, u32[]{:S(2)}) collective-permute-start(bf16[1,16,2048]{2,1,0:T(8,128)(2,1)S(1)} %get-tuple-element.6), channel_id=1, source_target_pairs={{0,4},{2,6},{4,0},{6,2},{8,12},{10,14},{12,8},{14,10},{1,5},{3,7},... | collective-permute-start | bytes 196616 | tf_op jit(solution)/shard_map/ppermute | solution.py:25
  88.5 1.8 %collective-permute-start.23 = (bf16[1,16,2048]{2,1,0:T(8,128)(2,1)S(1)}, bf16[1,16,2048]{2,1,0:T(8,128)(2,1)S(1)}, u32[]{:S(2)}, u32[]{:S(2)}) collective-permute-start(bf16[1,16,2048]{2,1,0:T(8,128)(2,1)S(1)} %get-tuple-element.7), channel_id=1, source_target_pairs={{0,12},{2,14},{4,8},{6,10},{8,4},{10,6},{12,0},{14,2},{1,13},{3,15... | collective-permute-start | bytes 196616 | tf_op jit(solution)/shard_map/ppermute | solution.py:25
  90.3 0.8 collective-permute-start.22
  91.0 1.1 %collective-permute-done.26 = bf16[1,16,2048]{2,1,0:T(8,128)(2,1)S(1)} collective-permute-done((bf16[1,16,2048]{2,1,0:T(8,128)(2,1)S(1)}, bf16[1,16,2048]{2,1,0:T(8,128)(2,1)S(1)}, u32[]{:S(2)}, u32[]{:S(2)}) %collective-permute-start.26) | collective-permute-done | bytes 65568 | tf_op jit(solution)/shard_map/ppermute | solution.py:25
  92.4 2.2 %collective-permute-done.23 = bf16[1,16,2048]{2,1,0:T(8,128)(2,1)S(1)} collective-permute-done((bf16[1,16,2048]{2,1,0:T(8,128)(2,1)S(1)}, bf16[1,16,2048]{2,1,0:T(8,128)(2,1)S(1)}, u32[]{:S(2)}, u32[]{:S(2)}) %collective-permute-start.23) | collective-permute-done | bytes 65568 | tf_op jit(solution)/shard_map/ppermute | solution.py:25
  94.6 1.4 %collective-permute-done.22 = bf16[1,16,2048]{2,1,0:T(8,128)(2,1)S(1)} collective-permute-done((bf16[1,16,2048]{2,1,0:T(8,128)(2,1)S(1)}, bf16[1,16,2048]{2,1,0:T(8,128)(2,1)S(1)}, u32[]{:S(2)}, u32[]{:S(2)}) %collective-permute-start.22) | collective-permute-done | bytes 65568 | tf_op jit(solution)/shard_map/ppermute | solution.py:25
  96.0 0.7 pad_maximum_fusion.2
  (59 shorter events, 2.2 us)
Async XLA Ops:
  0.6 0.9 copy-start
  3.9 10.1 %collective-permute-start.8 = (bf16[4,256,128]{2,1,0:T(8,128)(2,1)S(1)}, bf16[4,256,128]{2,1,0:T(8,128)(2,1)S(1)}, u32[]{:S(2)}, u32[]{:S(2)}) collective-permute-start(bf16[4,256,128]{2,1,0:T(8,128)(2,1)S(1)} %fusion.19), channel_id=1, source_target_pairs={{0,2},{2,0},{4,6},{6,4},{8,10},{10,8},{12,14},{14,12},{1,3},{3,1},... | collective-permute-start | bytes 786440 | tf_op jit(solution)/shard_map/ppermute | solution.py:25
  9.3 9.7 %collective-permute-start = (bf16[4,256,128]{2,1,0:T(8,128)(2,1)S(1)}, bf16[4,256,128]{2,1,0:T(8,128)(2,1)S(1)}, u32[]{:S(2)}, u32[]{:S(2)}) collective-permute-start(bf16[4,256,128]{2,1,0:T(8,128)(2,1)S(1)} %fusion.18), channel_id=1, source_target_pairs={{0,2},{2,0},{4,6},{6,4},{8,10},{10,8},{12,14},{14,12},{1,3},{3,1},... | collective-permute-start | bytes 786440 | tf_op jit(solution)/shard_map/ppermute | solution.py:25
  14.2 9.2 %collective-permute-start.9 = (bf16[1,256,128]{2,1,0:T(8,128)(2,1)S(1)}, bf16[1,256,128]{2,1,0:T(8,128)(2,1)S(1)}, u32[]{:S(2)}, u32[]{:S(2)}) collective-permute-start(bf16[1,256,128]{2,1,0:T(8,128)(2,1)S(1)} %get-tuple-element.19), channel_id=1, source_target_pairs={{0,4},{2,6},{4,0},{6,2},{8,12},{10,14},{12,8},{14,10},{1,5},{3,7},... | collective-permute-start | bytes 196616 | tf_op jit(solution)/shard_map/ppermute | solution.py:25
  16.4 7.1 %collective-permute-start.11 = (bf16[1,256,128]{2,1,0:T(8,128)(2,1)S(1)}, bf16[1,256,128]{2,1,0:T(8,128)(2,1)S(1)}, u32[]{:S(2)}, u32[]{:S(2)}) collective-permute-start(bf16[1,256,128]{2,1,0:T(8,128)(2,1)S(1)} %get-tuple-element.20), channel_id=1, source_target_pairs={{0,12},{2,14},{4,8},{6,10},{8,4},{10,6},{12,0},{14,2},{1,13},{3,15... | collective-permute-start | bytes 196616 | tf_op jit(solution)/shard_map/ppermute | solution.py:25
  18.8 8.4 %collective-permute-start.10 = (bf16[1,256,128]{2,1,0:T(8,128)(2,1)S(1)}, bf16[1,256,128]{2,1,0:T(8,128)(2,1)S(1)}, u32[]{:S(2)}, u32[]{:S(2)}) collective-permute-start(bf16[1,256,128]{2,1,0:T(8,128)(2,1)S(1)} %get-tuple-element.21), channel_id=1, source_target_pairs={{0,8},{2,10},{4,12},{6,14},{8,0},{10,2},{12,4},{14,6},{1,9},{3,11}... | collective-permute-start | bytes 196616 | tf_op jit(solution)/shard_map/ppermute | solution.py:25
  19.1 8.7 %collective-permute-start.1 = (bf16[1,256,128]{2,1,0:T(8,128)(2,1)S(1)}, bf16[1,256,128]{2,1,0:T(8,128)(2,1)S(1)}, u32[]{:S(2)}, u32[]{:S(2)}) collective-permute-start(bf16[1,256,128]{2,1,0:T(8,128)(2,1)S(1)} %get-tuple-element.14), channel_id=1, source_target_pairs={{0,4},{2,6},{4,0},{6,2},{8,12},{10,14},{12,8},{14,10},{1,5},{3,7},... | collective-permute-start | bytes 196616 | tf_op jit(solution)/shard_map/ppermute | solution.py:25
  20.9 10.8 %collective-permute-start.3 = (bf16[1,256,128]{2,1,0:T(8,128)(2,1)S(1)}, bf16[1,256,128]{2,1,0:T(8,128)(2,1)S(1)}, u32[]{:S(2)}, u32[]{:S(2)}) collective-permute-start(bf16[1,256,128]{2,1,0:T(8,128)(2,1)S(1)} %get-tuple-element.15), channel_id=1, source_target_pairs={{0,12},{2,14},{4,8},{6,10},{8,4},{10,6},{12,0},{14,2},{1,13},{3,15... | collective-permute-start | bytes 196616 | tf_op jit(solution)/shard_map/ppermute | solution.py:25
  23.4 8.9 %collective-permute-start.2 = (bf16[1,256,128]{2,1,0:T(8,128)(2,1)S(1)}, bf16[1,256,128]{2,1,0:T(8,128)(2,1)S(1)}, u32[]{:S(2)}, u32[]{:S(2)}) collective-permute-start(bf16[1,256,128]{2,1,0:T(8,128)(2,1)S(1)} %get-tuple-element.16), channel_id=1, source_target_pairs={{0,8},{2,10},{4,12},{6,14},{8,0},{10,2},{12,4},{14,6},{1,9},{3,11}... | collective-permute-start | bytes 196616 | tf_op jit(solution)/shard_map/ppermute | solution.py:25
  27.3 8.2 %collective-permute-start.14 = (bf16[1,256,128]{2,1,0:T(8,128)(2,1)S(1)}, bf16[1,256,128]{2,1,0:T(8,128)(2,1)S(1)}, u32[]{:S(2)}, u32[]{:S(2)}) collective-permute-start(bf16[1,256,128]{2,1,0:T(8,128)(2,1)S(1)} %multiply_convert_fusion), channel_id=1, source_target_pairs={{0,4},{2,6},{4,0},{6,2},{8,12},{10,14},{12,8},{14,10},{1,5},{3,7},... | collective-permute-start | bytes 196616 | tf_op jit(solution)/shard_map/ppermute | solution.py:25
  27.4 9.5 %collective-permute-start.13 = (bf16[1,256,128]{2,1,0:T(8,128)(2,1)S(1)}, bf16[1,256,128]{2,1,0:T(8,128)(2,1)S(1)}, u32[]{:S(2)}, u32[]{:S(2)}) collective-permute-start(bf16[1,256,128]{2,1,0:T(8,128)(2,1)S(1)} %multiply_convert_fusion), channel_id=1, source_target_pairs={{0,8},{2,10},{4,12},{6,14},{8,0},{10,2},{12,4},{14,6},{1,9},{3,11}... | collective-permute-start | bytes 196616 | tf_op jit(solution)/shard_map/ppermute | solution.py:25
  27.8 9.1 %collective-permute-start.12 = (bf16[1,256,128]{2,1,0:T(8,128)(2,1)S(1)}, bf16[1,256,128]{2,1,0:T(8,128)(2,1)S(1)}, u32[]{:S(2)}, u32[]{:S(2)}) collective-permute-start(bf16[1,256,128]{2,1,0:T(8,128)(2,1)S(1)} %multiply_convert_fusion), channel_id=1, source_target_pairs={{0,12},{2,14},{4,8},{6,10},{8,4},{10,6},{12,0},{14,2},{1,13},{3,15... | collective-permute-start | bytes 196616 | tf_op jit(solution)/shard_map/ppermute | solution.py:25
  32.4 6.1 %collective-permute-start.6 = (bf16[1,256,128]{2,1,0:T(8,128)(2,1)S(1)}, bf16[1,256,128]{2,1,0:T(8,128)(2,1)S(1)}, u32[]{:S(2)}, u32[]{:S(2)}) collective-permute-start(bf16[1,256,128]{2,1,0:T(8,128)(2,1)S(1)} %multiply_convert_fusion.1), channel_id=1, source_target_pairs={{0,4},{2,6},{4,0},{6,2},{8,12},{10,14},{12,8},{14,10},{1,5},{3,7},... | collective-permute-start | bytes 196616 | tf_op jit(solution)/shard_map/ppermute | solution.py:25
  32.5 7.3 %collective-permute-start.5 = (bf16[1,256,128]{2,1,0:T(8,128)(2,1)S(1)}, bf16[1,256,128]{2,1,0:T(8,128)(2,1)S(1)}, u32[]{:S(2)}, u32[]{:S(2)}) collective-permute-start(bf16[1,256,128]{2,1,0:T(8,128)(2,1)S(1)} %multiply_convert_fusion.1), channel_id=1, source_target_pairs={{0,8},{2,10},{4,12},{6,14},{8,0},{10,2},{12,4},{14,6},{1,9},{3,11}... | collective-permute-start | bytes 196616 | tf_op jit(solution)/shard_map/ppermute | solution.py:25
  35.5 6.1 %collective-permute-start.4 = (bf16[1,256,128]{2,1,0:T(8,128)(2,1)S(1)}, bf16[1,256,128]{2,1,0:T(8,128)(2,1)S(1)}, u32[]{:S(2)}, u32[]{:S(2)}) collective-permute-start(bf16[1,256,128]{2,1,0:T(8,128)(2,1)S(1)} %multiply_convert_fusion.1), channel_id=1, source_target_pairs={{0,12},{2,14},{4,8},{6,10},{8,4},{10,6},{12,0},{14,2},{1,13},{3,15... | collective-permute-start | bytes 196616 | tf_op jit(solution)/shard_map/ppermute | solution.py:25
  36.9 9.1 %copy-start.1 = (bf16[512,4096]{1,0:T(8,128)(2,1)S(1)}, bf16[512,4096]{1,0:T(8,128)(2,1)}, u32[]{:S(2)}) copy-start(bf16[512,4096]{1,0:T(8,128)(2,1)} %param.2) | copy-start | bytes 12582916
  36.9 8.9 %collective-permute-start.15 = (bf16[4,256,128]{2,1,0:T(8,128)(2,1)S(1)}, bf16[4,256,128]{2,1,0:T(8,128)(2,1)S(1)}, u32[]{:S(2)}, u32[]{:S(2)}) collective-permute-start(bf16[4,256,128]{2,1,0:T(8,128)(2,1)S(1)} %maximum_bitcast_fusion.1), channel_id=1, source_target_pairs={{0,2},{2,0},{4,6},{6,4},{8,10},{10,8},{12,14},{14,12},{1,3},{3,1},... | collective-permute-start | bytes 786440 | tf_op jit(solution)/shard_map/ppermute | solution.py:25
  41.6 7.4 %collective-permute-start.7 = (bf16[4,256,128]{2,1,0:T(8,128)(2,1)S(1)}, bf16[4,256,128]{2,1,0:T(8,128)(2,1)S(1)}, u32[]{:S(2)}, u32[]{:S(2)}) collective-permute-start(bf16[4,256,128]{2,1,0:T(8,128)(2,1)S(1)} %maximum_bitcast_fusion), channel_id=1, source_target_pairs={{0,2},{2,0},{4,6},{6,4},{8,10},{10,8},{12,14},{14,12},{1,3},{3,1},... | collective-permute-start | bytes 786440 | tf_op jit(solution)/shard_map/ppermute | solution.py:25
  49.8 17.5 %copy-start.4 = (f32[512,128]{1,0:T(8,128)}, f32[512,128]{1,0:T(8,128)S(1)}, u32[]{:S(2)}) copy-start(f32[512,128]{1,0:T(8,128)S(1)} %fusion.15.mine_ref) | copy-start | bytes 786436
  49.8 1.6 %collective-permute-start.16 = (f32[512,128]{1,0:T(8,128)S(1)}, f32[512,128]{1,0:T(8,128)S(1)}, u32[]{:S(2)}, u32[]{:S(2)}) collective-permute-start(f32[512,128]{1,0:T(8,128)S(1)} %fusion.15.mine_ref), channel_id=1, source_target_pairs={{0,1},{1,0},{2,3},{3,2},{4,5},{5,4},{6,7},{7,6},{8,9},{9,8},{10,11... | collective-permute-start | bytes 786440 | tf_op jit(solution)/shard_map/ppermute | solution.py:25
  51.4 15.9 %copy-start.5 = (f32[512,128]{1,0:T(8,128)}, f32[512,128]{1,0:T(8,128)S(1)}, u32[]{:S(2)}) copy-start(f32[512,128]{1,0:T(8,128)S(1)} %collective-permute-done.16.other_ref) | copy-start | bytes 786436
  52.0 4.3 %collective-permute-start.17 = (f32[128,128]{1,0:T(8,128)S(1)}, f32[128,128]{1,0:T(8,128)S(1)}, u32[]{:S(2)}, u32[]{:S(2)}) collective-permute-start(f32[128,128]{1,0:T(8,128)S(1)} %fusion.22), channel_id=1, source_target_pairs={{0,2},{2,0},{4,6},{6,4},{8,10},{10,8},{12,14},{14,12},{1,3},{3,1},... | collective-permute-start | bytes 196616 | tf_op jit(solution)/shard_map/ppermute | solution.py:25
  56.4 4.3 %collective-permute-start.18 = (f32[128,128]{1,0:T(8,128)S(1)}, f32[128,128]{1,0:T(8,128)S(1)}, u32[]{:S(2)}, u32[]{:S(2)}) collective-permute-start(f32[128,128]{1,0:T(8,128)S(1)} %add.128), channel_id=1, source_target_pairs={{0,4},{2,6},{4,0},{6,2},{8,12},{10,14},{12,8},{14,10},{1,5},{3,7},... | collective-permute-start | bytes 196616 | tf_op jit(solution)/shard_map/ppermute | solution.py:25
  60.7 5.9 %collective-permute-start.19 = (f32[128,128]{1,0:T(8,128)S(1)}, f32[128,128]{1,0:T(8,128)S(1)}, u32[]{:S(2)}, u32[]{:S(2)}) collective-permute-start(f32[128,128]{1,0:T(8,128)S(1)} %add.129), channel_id=1, source_target_pairs={{0,8},{2,10},{4,12},{6,14},{8,0},{10,2},{12,4},{14,6},{1,9},{3,11}... | collective-permute-start | bytes 196616 | tf_op jit(solution)/shard_map/ppermute | solution.py:25
  72.1 2.9 %copy-start.2 = (bf16[512,4096]{1,0:T(8,128)(2,1)S(1)}, bf16[512,4096]{1,0:T(8,128)(2,1)}, u32[]{:S(2)}) copy-start(bf16[512,4096]{1,0:T(8,128)(2,1)} %param.2) | copy-start | bytes 12582916
  72.1 2.9 %copy-start.3 = (bf16[512,256]{1,0:T(8,128)(2,1)S(1)}, bf16[512,256]{1,0:T(8,128)(2,1)}, u32[]{:S(2)}) copy-start(bf16[512,256]{1,0:T(8,128)(2,1)} %get-tuple-element.5) | copy-start | bytes 786436
  75.9 7.8 %collective-permute-start.24 = (bf16[4,16,2048]{2,1,0:T(8,128)(2,1)S(1)}, bf16[4,16,2048]{2,1,0:T(8,128)(2,1)S(1)}, u32[]{:S(2)}, u32[]{:S(2)}) collective-permute-start(bf16[4,16,2048]{2,1,0:T(8,128)(2,1)S(1)} %fusion.21), channel_id=1, source_target_pairs={{0,2},{2,0},{4,6},{6,4},{8,10},{10,8},{12,14},{14,12},{1,3},{3,1},... | collective-permute-start | bytes 786440 | tf_op jit(solution)/shard_map/ppermute | solution.py:25
  77.7 9.7 %collective-permute-start.20 = (bf16[4,16,2048]{2,1,0:T(8,128)(2,1)S(1)}, bf16[4,16,2048]{2,1,0:T(8,128)(2,1)S(1)}, u32[]{:S(2)}, u32[]{:S(2)}) collective-permute-start(bf16[4,16,2048]{2,1,0:T(8,128)(2,1)S(1)} %fusion.20), channel_id=1, source_target_pairs={{0,2},{2,0},{4,6},{6,4},{8,10},{10,8},{12,14},{14,12},{1,3},{3,1},... | collective-permute-start | bytes 786440 | tf_op jit(solution)/shard_map/ppermute | solution.py:25
  83.8 6.5 %collective-permute-start.25 = (bf16[1,16,2048]{2,1,0:T(8,128)(2,1)S(1)}, bf16[1,16,2048]{2,1,0:T(8,128)(2,1)S(1)}, u32[]{:S(2)}, u32[]{:S(2)}) collective-permute-start(bf16[1,16,2048]{2,1,0:T(8,128)(2,1)S(1)} %get-tuple-element.9), channel_id=1, source_target_pairs={{0,4},{2,6},{4,0},{6,2},{8,12},{10,14},{12,8},{14,10},{1,5},{3,7},... | collective-permute-start | bytes 196616 | tf_op jit(solution)/shard_map/ppermute | solution.py:25
  84.0 7.1 %collective-permute-start.27 = (bf16[1,16,2048]{2,1,0:T(8,128)(2,1)S(1)}, bf16[1,16,2048]{2,1,0:T(8,128)(2,1)S(1)}, u32[]{:S(2)}, u32[]{:S(2)}) collective-permute-start(bf16[1,16,2048]{2,1,0:T(8,128)(2,1)S(1)} %get-tuple-element.10), channel_id=1, source_target_pairs={{0,12},{2,14},{4,8},{6,10},{8,4},{10,6},{12,0},{14,2},{1,13},{3,15... | collective-permute-start | bytes 196616 | tf_op jit(solution)/shard_map/ppermute | solution.py:25
  85.7 6.5 %collective-permute-start.26 = (bf16[1,16,2048]{2,1,0:T(8,128)(2,1)S(1)}, bf16[1,16,2048]{2,1,0:T(8,128)(2,1)S(1)}, u32[]{:S(2)}, u32[]{:S(2)}) collective-permute-start(bf16[1,16,2048]{2,1,0:T(8,128)(2,1)S(1)} %get-tuple-element.11), channel_id=1, source_target_pairs={{0,8},{2,10},{4,12},{6,14},{8,0},{10,2},{12,4},{14,6},{1,9},{3,11}... | collective-permute-start | bytes 196616 | tf_op jit(solution)/shard_map/ppermute | solution.py:25
  87.5 4.9 %collective-permute-start.21 = (bf16[1,16,2048]{2,1,0:T(8,128)(2,1)S(1)}, bf16[1,16,2048]{2,1,0:T(8,128)(2,1)S(1)}, u32[]{:S(2)}, u32[]{:S(2)}) collective-permute-start(bf16[1,16,2048]{2,1,0:T(8,128)(2,1)S(1)} %get-tuple-element.6), channel_id=1, source_target_pairs={{0,4},{2,6},{4,0},{6,2},{8,12},{10,14},{12,8},{14,10},{1,5},{3,7},... | collective-permute-start | bytes 196616 | tf_op jit(solution)/shard_map/ppermute | solution.py:25
  88.5 6.1 %collective-permute-start.23 = (bf16[1,16,2048]{2,1,0:T(8,128)(2,1)S(1)}, bf16[1,16,2048]{2,1,0:T(8,128)(2,1)S(1)}, u32[]{:S(2)}, u32[]{:S(2)}) collective-permute-start(bf16[1,16,2048]{2,1,0:T(8,128)(2,1)S(1)} %get-tuple-element.7), channel_id=1, source_target_pairs={{0,12},{2,14},{4,8},{6,10},{8,4},{10,6},{12,0},{14,2},{1,13},{3,15... | collective-permute-start | bytes 196616 | tf_op jit(solution)/shard_map/ppermute | solution.py:25
  90.3 5.7 %collective-permute-start.22 = (bf16[1,16,2048]{2,1,0:T(8,128)(2,1)S(1)}, bf16[1,16,2048]{2,1,0:T(8,128)(2,1)S(1)}, u32[]{:S(2)}, u32[]{:S(2)}) collective-permute-start(bf16[1,16,2048]{2,1,0:T(8,128)(2,1)S(1)} %get-tuple-element.8), channel_id=1, source_target_pairs={{0,8},{2,10},{4,12},{6,14},{8,0},{10,2},{12,4},{14,6},{1,9},{3,11}... | collective-permute-start | bytes 196616 | tf_op jit(solution)/shard_map/ppermute | solution.py:25

commit v4 on v3

--- a/solution.py
+++ b/solution.py
@@ -100,10 +100,13 @@
 UPDATES = 4
 LOOSE_UPDATES = 2
 CLOSE = 1e-5
-
-
-def basis_kernel(total_cols, root_rows, gram_ref, mine_ref, other_ref, *refs):
-    basis_ref, pair_ref, work_ref, inverse_ref = refs
+TILE = 1024
+
+
+def basis_kernel(
+    total_cols, root_rows, gram_ref, mine_ref, other_ref, slab_ref,
+    basis_ref, product_ref, work_ref, inverse_ref,
+):
     width = gram_ref.shape[0]
     row = lax.broadcasted_iota(jnp.int32, (width, width), 0)
     col = lax.broadcasted_iota(jnp.int32, (width, width), 1)
@@ -153,26 +156,33 @@
     basis = matmul_t(sketch, inverse_ref[...]) * root_rows
     basis_ref[...] = basis
     high = basis.astype(jnp.bfloat16)
-    pair_ref[:, :width] = high
-    pair_ref[:, width:] = (basis - high.astype(jnp.float32)).astype(jnp.bfloat16)
-
-
-def make_basis(gram, mine, other, total_cols, root_rows):
+    low = (basis - high.astype(jnp.float32)).astype(jnp.bfloat16)
+    pair = jnp.concatenate([high, low], axis=1).T
+    for start in range(0, slab_ref.shape[1], TILE):
+        tile = slab_ref[:, start : start + TILE]
+        both = lax.dot_general(
+            pair, tile, (((1,), (0,)), ((), ())), preferred_element_type=jnp.float32
+        )
+        product_ref[:, start : start + TILE] = both[:width] + both[width:]
+
+
+def make_basis(gram, mine, other, slab, total_cols, root_rows):
     rows, width = mine.shape
     return pl.pallas_call(
         functools.partial(basis_kernel, total_cols, root_rows),
         out_shape=(
             jax.ShapeDtypeStruct((rows, width), jnp.float32),
-            jax.ShapeDtypeStruct((rows, 2 * width), jnp.bfloat16),
+            jax.ShapeDtypeStruct((width, slab.shape[1]), jnp.float32),
         ),
-        in_specs=[pl.BlockSpec(memory_space=pltpu.VMEM)] * 3,
+        in_specs=[pl.BlockSpec(memory_space=pltpu.VMEM)] * 4,
         out_specs=[pl.BlockSpec(memory_space=pltpu.VMEM)] * 2,
         scratch_shapes=[
             pltpu.VMEM((width, width), jnp.float32),
             pltpu.VMEM((width, width), jnp.float32),
         ],
+        compiler_params=pltpu.CompilerParams(vmem_limit_bytes=24 * 2**20),
         name="make_basis",
-    )(gram, mine, other)
+    )(gram, mine, other, slab)
 
 
 def per_device(activations, start_sketch):
@@ -208,17 +218,14 @@
         sketch, sketch, (((0,), (0,)), ((), ())), precision=lax.Precision.HIGHEST
     )
     gram = exchange_sum(local_gram, "row")
-    basis, pair = make_basis(gram, partial_sketch, other_sketch, total_cols, root_rows)
+    basis, local_proj = make_basis(
+        gram, partial_sketch, other_sketch, activations, total_cols, root_rows
+    )
 
     pieces = []
     for span in spans:
-        local_pair = lax.dot_general(
-            pair, activations[:, span], (((0,), (0,)), ((), ())), preferred_element_type=jnp.float32
-        )
-        local_proj = local_pair[:width] + local_pair[width:]
-        pieces.append(
-            scatter_sum(local_proj.reshape(parts, width // parts, cols_chunk), "row") / total_rows
-        )
+        blocks = local_proj[:, span].reshape(parts, width // parts, cols_chunk)
+        pieces.append(scatter_sum(blocks, "row") / total_rows)
     return (basis, jnp.concatenate(pieces, axis=1))
 
 

time: 97 us -> 92.3 us (0.952)
  matrix products: 9.95 us -> 6.68 us
    dot_general x2 -> x0, matrix products: 3.27 us -> none  [per_device(): lax.dot_general(pair, activations[:, span], (((0,), (0,)), ((), ())), pre...]
where the time goes in v4:
time: 92.3 us; the launch traced here: 92.1 us
  waiting for transfers between devices  40.5 us (44%)
  starting transfers between devices  36.7 us (40%)
  matrix products  6.68 us (7%)
  Pallas kernels  4.43 us (5%)
  other arithmetic  1.44 us (2%)
  local copies, waits for them, and re-layouts  1.37 us (1%)
  between operations  0.94 us (1%)
    ppermute x28, waiting for transfers between devices, swap(): return lax.ppermute(value, axis, [(i, i ^ distance) for i in range(size)])  40.5 us
    ppermute x28, starting transfers between devices, swap(): return lax.ppermute(value, axis, [(i, i ^ distance) for i in range(size)])  36.7 us
    dot_general x2, matrix products, per_device(): lax.dot_general(activations[:, span], start_sketch, (((0,), (0,)), ((), (...  4.65 us
    pallas_call x1, Pallas kernels, make_basis(): pl.pallas_call(functools.partial(basis_kernel, total_cols, root_rows), ou...  4.43 us
  transfers between devices with their start and end apart: 28, of which 16 were waited for; matrix products, arithmetic and copies ran while one was open for 4% of the time, Pallas kernels for 0%

profile of v4, /device:TPU:0, one launch (start us, length us, event | category | flops | bytes accessed | tf_op | source)
XLA Modules:
  0.0 92.1 jit_solution(10817155659932274800)
XLA Ops:
  0.7 0.9 copy-done
  1.5 2.3 %fusion.2 = f32[2048,128]{1,0:T(8,128)S(1)} fusion(bf16[512,128]{1,0:T(8,128)(2,1)S(1)} %copy-done, bf16[512,4096]{1,0:T(8,128)(2,1)} %slab_ref.1), kind=kOutput, calls=%fused_computation.2 | convolution fusion | flops 268435456 | bytes 3276800 | tf_op jit(solution)/shard_map/dot_general | solution.py:201
  3.9 3.0 %collective-permute-start.8 = (bf16[4,256,128]{2,1,0:T(8,128)(2,1)S(1)}, bf16[4,256,128]{2,1,0:T(8,128)(2,1)S(1)}, u32[]{:S(2)}, u32[]{:S(2)}) collective-permute-start(bf16[4,256,128]{2,1,0:T(8,128)(2,1)S(1)} %fusion.15), channel_id=1, source_target_pairs={{0,2},{2,0},{4,6},{6,4},{8,10},{10,8},{12,14},{14,12},{1,3},{3,1},... | collective-permute-start | bytes 786440 | tf_op jit(solution)/shard_map/ppermute | solution.py:25
  6.9 2.3 %fusion.6 = f32[2048,128]{1,0:T(8,128)S(1)} fusion(bf16[512,128]{1,0:T(8,128)(2,1)S(1)} %copy-done, bf16[512,4096]{1,0:T(8,128)(2,1)} %slab_ref.1), kind=kOutput, calls=%fused_computation.6 | convolution fusion | flops 268435456 | bytes 3276800 | tf_op jit(solution)/shard_map/dot_general | solution.py:201
  9.4 4.6 %collective-permute-done.8 = bf16[4,256,128]{2,1,0:T(8,128)(2,1)S(1)} collective-permute-done((bf16[4,256,128]{2,1,0:T(8,128)(2,1)S(1)}, bf16[4,256,128]{2,1,0:T(8,128)(2,1)S(1)}, u32[]{:S(2)}, u32[]{:S(2)}) %collective-permute-start.8) | collective-permute-done | bytes 262176 | tf_op jit(solution)/shard_map/ppermute | solution.py:25
  14.2 2.2 %collective-permute-start.9 = (bf16[1,256,128]{2,1,0:T(8,128)(2,1)S(1)}, bf16[1,256,128]{2,1,0:T(8,128)(2,1)S(1)}, u32[]{:S(2)}, u32[]{:S(2)}) collective-permute-start(bf16[1,256,128]{2,1,0:T(8,128)(2,1)S(1)} %get-tuple-element.21), channel_id=1, source_target_pairs={{0,4},{2,6},{4,0},{6,2},{8,12},{10,14},{12,8},{14,10},{1,5},{3,7},... | collective-permute-start | bytes 196616 | tf_op jit(solution)/shard_map/ppermute | solution.py:25
  16.4 2.5 %collective-permute-start.11 = (bf16[1,256,128]{2,1,0:T(8,128)(2,1)S(1)}, bf16[1,256,128]{2,1,0:T(8,128)(2,1)S(1)}, u32[]{:S(2)}, u32[]{:S(2)}) collective-permute-start(bf16[1,256,128]{2,1,0:T(8,128)(2,1)S(1)} %get-tuple-element.22), channel_id=1, source_target_pairs={{0,12},{2,14},{4,8},{6,10},{8,4},{10,6},{12,0},{14,2},{1,13},{3,15... | collective-permute-start | bytes 196616 | tf_op jit(solution)/shard_map/ppermute | solution.py:25
  18.8 0.1 collective-permute-start.10
  19.1 1.9 %collective-permute-start.1 = (bf16[1,256,128]{2,1,0:T(8,128)(2,1)S(1)}, bf16[1,256,128]{2,1,0:T(8,128)(2,1)S(1)}, u32[]{:S(2)}, u32[]{:S(2)}) collective-permute-start(bf16[1,256,128]{2,1,0:T(8,128)(2,1)S(1)} %get-tuple-element.16), channel_id=1, source_target_pairs={{0,4},{2,6},{4,0},{6,2},{8,12},{10,14},{12,8},{14,10},{1,5},{3,7},... | collective-permute-start | bytes 196616 | tf_op jit(solution)/shard_map/ppermute | solution.py:25
  20.9 2.5 %collective-permute-start.3 = (bf16[1,256,128]{2,1,0:T(8,128)(2,1)S(1)}, bf16[1,256,128]{2,1,0:T(8,128)(2,1)S(1)}, u32[]{:S(2)}, u32[]{:S(2)}) collective-permute-start(bf16[1,256,128]{2,1,0:T(8,128)(2,1)S(1)} %get-tuple-element.17), channel_id=1, source_target_pairs={{0,12},{2,14},{4,8},{6,10},{8,4},{10,6},{12,0},{14,2},{1,13},{3,15... | collective-permute-start | bytes 196616 | tf_op jit(solution)/shard_map/ppermute | solution.py:25
  23.4 3.8 %collective-permute-done.10 = bf16[1,256,128]{2,1,0:T(8,128)(2,1)S(1)} collective-permute-done((bf16[1,256,128]{2,1,0:T(8,128)(2,1)S(1)}, bf16[1,256,128]{2,1,0:T(8,128)(2,1)S(1)}, u32[]{:S(2)}, u32[]{:S(2)}) %collective-permute-start.10) | collective-permute-done | bytes 65568 | tf_op jit(solution)/shard_map/ppermute | solution.py:25
  27.4 0.4 collective-permute-start.13
  27.8 4.0 %collective-permute-start.12 = (bf16[1,256,128]{2,1,0:T(8,128)(2,1)S(1)}, bf16[1,256,128]{2,1,0:T(8,128)(2,1)S(1)}, u32[]{:S(2)}, u32[]{:S(2)}) collective-permute-start(bf16[1,256,128]{2,1,0:T(8,128)(2,1)S(1)} %multiply_convert_fusion), channel_id=1, source_target_pairs={{0,12},{2,14},{4,8},{6,10},{8,4},{10,6},{12,0},{14,2},{1,13},{3,15... | collective-permute-start | bytes 196616 | tf_op jit(solution)/shard_map/ppermute | solution.py:25
  31.8 0.6 collective-permute-done.2
  32.5 3.0 %collective-permute-start.5 = (bf16[1,256,128]{2,1,0:T(8,128)(2,1)S(1)}, bf16[1,256,128]{2,1,0:T(8,128)(2,1)S(1)}, u32[]{:S(2)}, u32[]{:S(2)}) collective-permute-start(bf16[1,256,128]{2,1,0:T(8,128)(2,1)S(1)} %multiply_convert_fusion.1), channel_id=1, source_target_pairs={{0,8},{2,10},{4,12},{6,14},{8,0},{10,2},{12,4},{14,6},{1,9},{3,11}... | collective-permute-start | bytes 196616 | tf_op jit(solution)/shard_map/ppermute | solution.py:25
  35.5 1.4 %collective-permute-start.4 = (bf16[1,256,128]{2,1,0:T(8,128)(2,1)S(1)}, bf16[1,256,128]{2,1,0:T(8,128)(2,1)S(1)}, u32[]{:S(2)}, u32[]{:S(2)}) collective-permute-start(bf16[1,256,128]{2,1,0:T(8,128)(2,1)S(1)} %multiply_convert_fusion.1), channel_id=1, source_target_pairs={{0,12},{2,14},{4,8},{6,10},{8,4},{10,6},{12,0},{14,2},{1,13},{3,15... | collective-permute-start | bytes 196616 | tf_op jit(solution)/shard_map/ppermute | solution.py:25
  36.9 1.6 %collective-permute-start.15 = (bf16[4,256,128]{2,1,0:T(8,128)(2,1)S(1)}, bf16[4,256,128]{2,1,0:T(8,128)(2,1)S(1)}, u32[]{:S(2)}, u32[]{:S(2)}) collective-permute-start(bf16[4,256,128]{2,1,0:T(8,128)(2,1)S(1)} %maximum_bitcast_fusion.1), channel_id=1, source_target_pairs={{0,2},{2,0},{4,6},{6,4},{8,10},{10,8},{12,14},{14,12},{1,3},{3,1},... | collective-permute-start | bytes 786440 | tf_op jit(solution)/shard_map/ppermute | solution.py:25
  38.5 1.3 %collective-permute-done.5 = bf16[1,256,128]{2,1,0:T(8,128)(2,1)S(1)} collective-permute-done((bf16[1,256,128]{2,1,0:T(8,128)(2,1)S(1)}, bf16[1,256,128]{2,1,0:T(8,128)(2,1)S(1)}, u32[]{:S(2)}, u32[]{:S(2)}) %collective-permute-start.5) | collective-permute-done | bytes 65568 | tf_op jit(solution)/shard_map/ppermute | solution.py:25
  39.8 1.7 %collective-permute-done.4 = bf16[1,256,128]{2,1,0:T(8,128)(2,1)S(1)} collective-permute-done((bf16[1,256,128]{2,1,0:T(8,128)(2,1)S(1)}, bf16[1,256,128]{2,1,0:T(8,128)(2,1)S(1)}, u32[]{:S(2)}, u32[]{:S(2)}) %collective-permute-start.4) | collective-permute-done | bytes 65568 | tf_op jit(solution)/shard_map/ppermute | solution.py:25
  41.6 1.6 %collective-permute-start.7 = (bf16[4,256,128]{2,1,0:T(8,128)(2,1)S(1)}, bf16[4,256,128]{2,1,0:T(8,128)(2,1)S(1)}, u32[]{:S(2)}, u32[]{:S(2)}) collective-permute-start(bf16[4,256,128]{2,1,0:T(8,128)(2,1)S(1)} %maximum_bitcast_fusion), channel_id=1, source_target_pairs={{0,2},{2,0},{4,6},{6,4},{8,10},{10,8},{12,14},{14,12},{1,3},{3,1},... | collective-permute-start | bytes 786440 | tf_op jit(solution)/shard_map/ppermute | solution.py:25
  43.2 2.6 %collective-permute-done.15 = bf16[4,256,128]{2,1,0:T(8,128)(2,1)S(1)} collective-permute-done((bf16[4,256,128]{2,1,0:T(8,128)(2,1)S(1)}, bf16[4,256,128]{2,1,0:T(8,128)(2,1)S(1)}, u32[]{:S(2)}, u32[]{:S(2)}) %collective-permute-start.15) | collective-permute-done | bytes 262176 | tf_op jit(solution)/shard_map/ppermute | solution.py:25
  46.0 0.7 fusion
  46.7 2.3 %collective-permute-done.7 = bf16[4,256,128]{2,1,0:T(8,128)(2,1)S(1)} collective-permute-done((bf16[4,256,128]{2,1,0:T(8,128)(2,1)S(1)}, bf16[4,256,128]{2,1,0:T(8,128)(2,1)S(1)}, u32[]{:S(2)}, u32[]{:S(2)}) %collective-permute-start.7) | collective-permute-done | bytes 262176 | tf_op jit(solution)/shard_map/ppermute | solution.py:25
  49.1 0.7 fusion.11.mine_ref
  49.9 1.5 %collective-permute-done.16.other_ref = f32[512,128]{1,0:T(8,128)S(1)} collective-permute-done((f32[512,128]{1,0:T(8,128)S(1)}, f32[512,128]{1,0:T(8,128)S(1)}, u32[]{:S(2)}, u32[]{:S(2)}) %collective-permute-start.16) | collective-permute-done | bytes 262176 | tf_op jit(solution)/shard_map/ppermute | solution.py:25
  51.4 0.6 fusion.18
  52.0 1.6 %collective-permute-start.17 = (f32[128,128]{1,0:T(8,128)S(1)}, f32[128,128]{1,0:T(8,128)S(1)}, u32[]{:S(2)}, u32[]{:S(2)}) collective-permute-start(f32[128,128]{1,0:T(8,128)S(1)} %fusion.18), channel_id=1, source_target_pairs={{0,2},{2,0},{4,6},{6,4},{8,10},{10,8},{12,14},{14,12},{1,3},{3,1},... | collective-permute-start | bytes 196616 | tf_op jit(solution)/shard_map/ppermute | solution.py:25
  53.6 2.8 %collective-permute-done.17 = f32[128,128]{1,0:T(8,128)S(1)} collective-permute-done((f32[128,128]{1,0:T(8,128)S(1)}, f32[128,128]{1,0:T(8,128)S(1)}, u32[]{:S(2)}, u32[]{:S(2)}) %collective-permute-start.17) | collective-permute-done | bytes 65568 | tf_op jit(solution)/shard_map/ppermute | solution.py:25
  56.4 0.7 collective-permute-start.18
  57.1 3.6 %collective-permute-done.18 = f32[128,128]{1,0:T(8,128)S(1)} collective-permute-done((f32[128,128]{1,0:T(8,128)S(1)}, f32[128,128]{1,0:T(8,128)S(1)}, u32[]{:S(2)}, u32[]{:S(2)}) %collective-permute-start.18) | collective-permute-done | bytes 65568 | tf_op jit(solution)/shard_map/ppermute | solution.py:25
  60.7 0.8 collective-permute-start.19
  61.5 5.1 %collective-permute-done.19 = f32[128,128]{1,0:T(8,128)S(1)} collective-permute-done((f32[128,128]{1,0:T(8,128)S(1)}, f32[128,128]{1,0:T(8,128)S(1)}, u32[]{:S(2)}, u32[]{:S(2)}) %collective-permute-start.19) | collective-permute-done | bytes 65568 | tf_op jit(solution)/shard_map/ppermute | solution.py:25
  66.7 4.4 %make_basis.1 = (f32[512,128]{1,0:T(8,128)}, f32[128,4096]{1,0:T(8,128)S(1)}) custom-call(f32[128,128]{1,0:T(8,128)S(1)} %add.124.gram_ref, f32[512,128]{1,0:T(8,128)S(1)} %fusion.11.mine_ref, f32[512,128]{1,0:T(8,128)S(1)} %collective-permute-done.16.other_ref, bf16[512,4096]{1,0:T(8,128)(2,1)S(1)} %copy-done.1), custom_call_target="tpu_custom_call" | custom-call | tf_op jit(solution)/shard_map/make_basis/pallas_call | solution.py:171
  71.1 0.1 fusion.23
  71.3 1.6 %collective-permute-start.20 = (bf16[4,16,2048]{2,1,0:T(8,128)(2,1)S(1)}, bf16[4,16,2048]{2,1,0:T(8,128)(2,1)S(1)}, u32[]{:S(2)}, u32[]{:S(2)}) collective-permute-start(bf16[4,16,2048]{2,1,0:T(8,128)(2,1)S(1)} %fusion.16), channel_id=1, source_target_pairs={{0,2},{2,0},{4,6},{6,4},{8,10},{10,8},{12,14},{14,12},{1,3},{3,1},... | collective-permute-start | bytes 786440 | tf_op jit(solution)/shard_map/ppermute | solution.py:25
  72.9 0.6 collective-permute-start.24
  73.5 5.6 %collective-permute-done.20 = bf16[4,16,2048]{2,1,0:T(8,128)(2,1)S(1)} collective-permute-done((bf16[4,16,2048]{2,1,0:T(8,128)(2,1)S(1)}, bf16[4,16,2048]{2,1,0:T(8,128)(2,1)S(1)}, u32[]{:S(2)}, u32[]{:S(2)}) %collective-permute-start.20) | collective-permute-done | bytes 262176 | tf_op jit(solution)/shard_map/ppermute | solution.py:25
  79.2 0.1 collective-permute-start.21
  79.3 1.8 %collective-permute-start.23 = (bf16[1,16,2048]{2,1,0:T(8,128)(2,1)S(1)}, bf16[1,16,2048]{2,1,0:T(8,128)(2,1)S(1)}, u32[]{:S(2)}, u32[]{:S(2)}) collective-permute-start(bf16[1,16,2048]{2,1,0:T(8,128)(2,1)S(1)} %get-tuple-element.9), channel_id=1, source_target_pairs={{0,12},{2,14},{4,8},{6,10},{8,4},{10,6},{12,0},{14,2},{1,13},{3,15... | collective-permute-start | bytes 196616 | tf_op jit(solution)/shard_map/ppermute | solution.py:25
  81.1 1.7 %collective-permute-start.22 = (bf16[1,16,2048]{2,1,0:T(8,128)(2,1)S(1)}, bf16[1,16,2048]{2,1,0:T(8,128)(2,1)S(1)}, u32[]{:S(2)}, u32[]{:S(2)}) collective-permute-start(bf16[1,16,2048]{2,1,0:T(8,128)(2,1)S(1)} %get-tuple-element.10), channel_id=1, source_target_pairs={{0,8},{2,10},{4,12},{6,14},{8,0},{10,2},{12,4},{14,6},{1,9},{3,11}... | collective-permute-start | bytes 196616 | tf_op jit(solution)/shard_map/ppermute | solution.py:25
  82.8 1.0 %collective-permute-start.25 = (bf16[1,16,2048]{2,1,0:T(8,128)(2,1)S(1)}, bf16[1,16,2048]{2,1,0:T(8,128)(2,1)S(1)}, u32[]{:S(2)}, u32[]{:S(2)}) collective-permute-start(bf16[1,16,2048]{2,1,0:T(8,128)(2,1)S(1)} %get-tuple-element.11), channel_id=1, source_target_pairs={{0,4},{2,6},{4,0},{6,2},{8,12},{10,14},{12,8},{14,10},{1,5},{3,7},... | collective-permute-start | bytes 196616 | tf_op jit(solution)/shard_map/ppermute | solution.py:25
  83.9 1.8 %collective-permute-start.27 = (bf16[1,16,2048]{2,1,0:T(8,128)(2,1)S(1)}, bf16[1,16,2048]{2,1,0:T(8,128)(2,1)S(1)}, u32[]{:S(2)}, u32[]{:S(2)}) collective-permute-start(bf16[1,16,2048]{2,1,0:T(8,128)(2,1)S(1)} %get-tuple-element.12), channel_id=1, source_target_pairs={{0,12},{2,14},{4,8},{6,10},{8,4},{10,6},{12,0},{14,2},{1,13},{3,15... | collective-permute-start | bytes 196616 | tf_op jit(solution)/shard_map/ppermute | solution.py:25
  85.6 0.8 collective-permute-start.26
  86.4 1.1 %collective-permute-done.22 = bf16[1,16,2048]{2,1,0:T(8,128)(2,1)S(1)} collective-permute-done((bf16[1,16,2048]{2,1,0:T(8,128)(2,1)S(1)}, bf16[1,16,2048]{2,1,0:T(8,128)(2,1)S(1)}, u32[]{:S(2)}, u32[]{:S(2)}) %collective-permute-start.22) | collective-permute-done | bytes 65568 | tf_op jit(solution)/shard_map/ppermute | solution.py:25
  87.6 0.2 collective-permute-done.25
  87.8 2.2 %collective-permute-done.27 = bf16[1,16,2048]{2,1,0:T(8,128)(2,1)S(1)} collective-permute-done((bf16[1,16,2048]{2,1,0:T(8,128)(2,1)S(1)}, bf16[1,16,2048]{2,1,0:T(8,128)(2,1)S(1)}, u32[]{:S(2)}, u32[]{:S(2)}) %collective-permute-start.27) | collective-permute-done | bytes 65568 | tf_op jit(solution)/shard_map/ppermute | solution.py:25
  89.9 1.4 %collective-permute-done.26 = bf16[1,16,2048]{2,1,0:T(8,128)(2,1)S(1)} collective-permute-done((bf16[1,16,2048]{2,1,0:T(8,128)(2,1)S(1)}, bf16[1,16,2048]{2,1,0:T(8,128)(2,1)S(1)}, u32[]{:S(2)}, u32[]{:S(2)}) %collective-permute-start.26) | collective-permute-done | bytes 65568 | tf_op jit(solution)/shard_map/ppermute | solution.py:25
  91.4 0.7 pad_maximum_fusion.2
  (48 shorter events, 1.4 us)
Async XLA Ops:
  0.6 0.9 copy-start
  3.9 10.1 %collective-permute-start.8 = (bf16[4,256,128]{2,1,0:T(8,128)(2,1)S(1)}, bf16[4,256,128]{2,1,0:T(8,128)(2,1)S(1)}, u32[]{:S(2)}, u32[]{:S(2)}) collective-permute-start(bf16[4,256,128]{2,1,0:T(8,128)(2,1)S(1)} %fusion.15), channel_id=1, source_target_pairs={{0,2},{2,0},{4,6},{6,4},{8,10},{10,8},{12,14},{14,12},{1,3},{3,1},... | collective-permute-start | bytes 786440 | tf_op jit(solution)/shard_map/ppermute | solution.py:25
  9.3 9.7 %collective-permute-start = (bf16[4,256,128]{2,1,0:T(8,128)(2,1)S(1)}, bf16[4,256,128]{2,1,0:T(8,128)(2,1)S(1)}, u32[]{:S(2)}, u32[]{:S(2)}) collective-permute-start(bf16[4,256,128]{2,1,0:T(8,128)(2,1)S(1)} %fusion.14), channel_id=1, source_target_pairs={{0,2},{2,0},{4,6},{6,4},{8,10},{10,8},{12,14},{14,12},{1,3},{3,1},... | collective-permute-start | bytes 786440 | tf_op jit(solution)/shard_map/ppermute | solution.py:25
  14.2 9.2 %collective-permute-start.9 = (bf16[1,256,128]{2,1,0:T(8,128)(2,1)S(1)}, bf16[1,256,128]{2,1,0:T(8,128)(2,1)S(1)}, u32[]{:S(2)}, u32[]{:S(2)}) collective-permute-start(bf16[1,256,128]{2,1,0:T(8,128)(2,1)S(1)} %get-tuple-element.21), channel_id=1, source_target_pairs={{0,4},{2,6},{4,0},{6,2},{8,12},{10,14},{12,8},{14,10},{1,5},{3,7},... | collective-permute-start | bytes 196616 | tf_op jit(solution)/shard_map/ppermute | solution.py:25
  16.4 7.1 %collective-permute-start.11 = (bf16[1,256,128]{2,1,0:T(8,128)(2,1)S(1)}, bf16[1,256,128]{2,1,0:T(8,128)(2,1)S(1)}, u32[]{:S(2)}, u32[]{:S(2)}) collective-permute-start(bf16[1,256,128]{2,1,0:T(8,128)(2,1)S(1)} %get-tuple-element.22), channel_id=1, source_target_pairs={{0,12},{2,14},{4,8},{6,10},{8,4},{10,6},{12,0},{14,2},{1,13},{3,15... | collective-permute-start | bytes 196616 | tf_op jit(solution)/shard_map/ppermute | solution.py:25
  18.8 8.4 %collective-permute-start.10 = (bf16[1,256,128]{2,1,0:T(8,128)(2,1)S(1)}, bf16[1,256,128]{2,1,0:T(8,128)(2,1)S(1)}, u32[]{:S(2)}, u32[]{:S(2)}) collective-permute-start(bf16[1,256,128]{2,1,0:T(8,128)(2,1)S(1)} %get-tuple-element.23), channel_id=1, source_target_pairs={{0,8},{2,10},{4,12},{6,14},{8,0},{10,2},{12,4},{14,6},{1,9},{3,11}... | collective-permute-start | bytes 196616 | tf_op jit(solution)/shard_map/ppermute | solution.py:25
  19.1 8.7 %collective-permute-start.1 = (bf16[1,256,128]{2,1,0:T(8,128)(2,1)S(1)}, bf16[1,256,128]{2,1,0:T(8,128)(2,1)S(1)}, u32[]{:S(2)}, u32[]{:S(2)}) collective-permute-start(bf16[1,256,128]{2,1,0:T(8,128)(2,1)S(1)} %get-tuple-element.16), channel_id=1, source_target_pairs={{0,4},{2,6},{4,0},{6,2},{8,12},{10,14},{12,8},{14,10},{1,5},{3,7},... | collective-permute-start | bytes 196616 | tf_op jit(solution)/shard_map/ppermute | solution.py:25
  20.9 10.8 %collective-permute-start.3 = (bf16[1,256,128]{2,1,0:T(8,128)(2,1)S(1)}, bf16[1,256,128]{2,1,0:T(8,128)(2,1)S(1)}, u32[]{:S(2)}, u32[]{:S(2)}) collective-permute-start(bf16[1,256,128]{2,1,0:T(8,128)(2,1)S(1)} %get-tuple-element.17), channel_id=1, source_target_pairs={{0,12},{2,14},{4,8},{6,10},{8,4},{10,6},{12,0},{14,2},{1,13},{3,15... | collective-permute-start | bytes 196616 | tf_op jit(solution)/shard_map/ppermute | solution.py:25
  23.4 8.9 %collective-permute-start.2 = (bf16[1,256,128]{2,1,0:T(8,128)(2,1)S(1)}, bf16[1,256,128]{2,1,0:T(8,128)(2,1)S(1)}, u32[]{:S(2)}, u32[]{:S(2)}) collective-permute-start(bf16[1,256,128]{2,1,0:T(8,128)(2,1)S(1)} %get-tuple-element.18), channel_id=1, source_target_pairs={{0,8},{2,10},{4,12},{6,14},{8,0},{10,2},{12,4},{14,6},{1,9},{3,11}... | collective-permute-start | bytes 196616 | tf_op jit(solution)/shard_map/ppermute | solution.py:25
  27.3 8.2 %collective-permute-start.14 = (bf16[1,256,128]{2,1,0:T(8,128)(2,1)S(1)}, bf16[1,256,128]{2,1,0:T(8,128)(2,1)S(1)}, u32[]{:S(2)}, u32[]{:S(2)}) collective-permute-start(bf16[1,256,128]{2,1,0:T(8,128)(2,1)S(1)} %multiply_convert_fusion), channel_id=1, source_target_pairs={{0,4},{2,6},{4,0},{6,2},{8,12},{10,14},{12,8},{14,10},{1,5},{3,7},... | collective-permute-start | bytes 196616 | tf_op jit(solution)/shard_map/ppermute | solution.py:25
  27.4 9.5 %collective-permute-start.13 = (bf16[1,256,128]{2,1,0:T(8,128)(2,1)S(1)}, bf16[1,256,128]{2,1,0:T(8,128)(2,1)S(1)}, u32[]{:S(2)}, u32[]{:S(2)}) collective-permute-start(bf16[1,256,128]{2,1,0:T(8,128)(2,1)S(1)} %multiply_convert_fusion), channel_id=1, source_target_pairs={{0,8},{2,10},{4,12},{6,14},{8,0},{10,2},{12,4},{14,6},{1,9},{3,11}... | collective-permute-start | bytes 196616 | tf_op jit(solution)/shard_map/ppermute | solution.py:25
  27.8 9.1 %collective-permute-start.12 = (bf16[1,256,128]{2,1,0:T(8,128)(2,1)S(1)}, bf16[1,256,128]{2,1,0:T(8,128)(2,1)S(1)}, u32[]{:S(2)}, u32[]{:S(2)}) collective-permute-start(bf16[1,256,128]{2,1,0:T(8,128)(2,1)S(1)} %multiply_convert_fusion), channel_id=1, source_target_pairs={{0,12},{2,14},{4,8},{6,10},{8,4},{10,6},{12,0},{14,2},{1,13},{3,15... | collective-permute-start | bytes 196616 | tf_op jit(solution)/shard_map/ppermute | solution.py:25
  32.4 6.1 %collective-permute-start.6 = (bf16[1,256,128]{2,1,0:T(8,128)(2,1)S(1)}, bf16[1,256,128]{2,1,0:T(8,128)(2,1)S(1)}, u32[]{:S(2)}, u32[]{:S(2)}) collective-permute-start(bf16[1,256,128]{2,1,0:T(8,128)(2,1)S(1)} %multiply_convert_fusion.1), channel_id=1, source_target_pairs={{0,4},{2,6},{4,0},{6,2},{8,12},{10,14},{12,8},{14,10},{1,5},{3,7},... | collective-permute-start | bytes 196616 | tf_op jit(solution)/shard_map/ppermute | solution.py:25
  32.5 7.3 %collective-permute-start.5 = (bf16[1,256,128]{2,1,0:T(8,128)(2,1)S(1)}, bf16[1,256,128]{2,1,0:T(8,128)(2,1)S(1)}, u32[]{:S(2)}, u32[]{:S(2)}) collective-permute-start(bf16[1,256,128]{2,1,0:T(8,128)(2,1)S(1)} %multiply_convert_fusion.1), channel_id=1, source_target_pairs={{0,8},{2,10},{4,12},{6,14},{8,0},{10,2},{12,4},{14,6},{1,9},{3,11}... | collective-permute-start | bytes 196616 | tf_op jit(solution)/shard_map/ppermute | solution.py:25
  35.5 6.1 %collective-permute-start.4 = (bf16[1,256,128]{2,1,0:T(8,128)(2,1)S(1)}, bf16[1,256,128]{2,1,0:T(8,128)(2,1)S(1)}, u32[]{:S(2)}, u32[]{:S(2)}) collective-permute-start(bf16[1,256,128]{2,1,0:T(8,128)(2,1)S(1)} %multiply_convert_fusion.1), channel_id=1, source_target_pairs={{0,12},{2,14},{4,8},{6,10},{8,4},{10,6},{12,0},{14,2},{1,13},{3,15... | collective-permute-start | bytes 196616 | tf_op jit(solution)/shard_map/ppermute | solution.py:25
  36.9 9.1 %copy-start.1 = (bf16[512,4096]{1,0:T(8,128)(2,1)S(1)}, bf16[512,4096]{1,0:T(8,128)(2,1)}, u32[]{:S(2)}) copy-start(bf16[512,4096]{1,0:T(8,128)(2,1)} %slab_ref.1) | copy-start | bytes 12582916
  36.9 8.9 %collective-permute-start.15 = (bf16[4,256,128]{2,1,0:T(8,128)(2,1)S(1)}, bf16[4,256,128]{2,1,0:T(8,128)(2,1)S(1)}, u32[]{:S(2)}, u32[]{:S(2)}) collective-permute-start(bf16[4,256,128]{2,1,0:T(8,128)(2,1)S(1)} %maximum_bitcast_fusion.1), channel_id=1, source_target_pairs={{0,2},{2,0},{4,6},{6,4},{8,10},{10,8},{12,14},{14,12},{1,3},{3,1},... | collective-permute-start | bytes 786440 | tf_op jit(solution)/shard_map/ppermute | solution.py:25
  41.6 7.4 %collective-permute-start.7 = (bf16[4,256,128]{2,1,0:T(8,128)(2,1)S(1)}, bf16[4,256,128]{2,1,0:T(8,128)(2,1)S(1)}, u32[]{:S(2)}, u32[]{:S(2)}) collective-permute-start(bf16[4,256,128]{2,1,0:T(8,128)(2,1)S(1)} %maximum_bitcast_fusion), channel_id=1, source_target_pairs={{0,2},{2,0},{4,6},{6,4},{8,10},{10,8},{12,14},{14,12},{1,3},{3,1},... | collective-permute-start | bytes 786440 | tf_op jit(solution)/shard_map/ppermute | solution.py:25
  49.8 1.6 %collective-permute-start.16 = (f32[512,128]{1,0:T(8,128)S(1)}, f32[512,128]{1,0:T(8,128)S(1)}, u32[]{:S(2)}, u32[]{:S(2)}) collective-permute-start(f32[512,128]{1,0:T(8,128)S(1)} %fusion.11.mine_ref), channel_id=1, source_target_pairs={{0,1},{1,0},{2,3},{3,2},{4,5},{5,4},{6,7},{7,6},{8,9},{9,8},{10,11... | collective-permute-start | bytes 786440 | tf_op jit(solution)/shard_map/ppermute | solution.py:25
  52.0 4.3 %collective-permute-start.17 = (f32[128,128]{1,0:T(8,128)S(1)}, f32[128,128]{1,0:T(8,128)S(1)}, u32[]{:S(2)}, u32[]{:S(2)}) collective-permute-start(f32[128,128]{1,0:T(8,128)S(1)} %fusion.18), channel_id=1, source_target_pairs={{0,2},{2,0},{4,6},{6,4},{8,10},{10,8},{12,14},{14,12},{1,3},{3,1},... | collective-permute-start | bytes 196616 | tf_op jit(solution)/shard_map/ppermute | solution.py:25
  56.4 4.3 %collective-permute-start.18 = (f32[128,128]{1,0:T(8,128)S(1)}, f32[128,128]{1,0:T(8,128)S(1)}, u32[]{:S(2)}, u32[]{:S(2)}) collective-permute-start(f32[128,128]{1,0:T(8,128)S(1)} %add.122), channel_id=1, source_target_pairs={{0,4},{2,6},{4,0},{6,2},{8,12},{10,14},{12,8},{14,10},{1,5},{3,7},... | collective-permute-start | bytes 196616 | tf_op jit(solution)/shard_map/ppermute | solution.py:25
  60.7 5.9 %collective-permute-start.19 = (f32[128,128]{1,0:T(8,128)S(1)}, f32[128,128]{1,0:T(8,128)S(1)}, u32[]{:S(2)}, u32[]{:S(2)}) collective-permute-start(f32[128,128]{1,0:T(8,128)S(1)} %add.123), channel_id=1, source_target_pairs={{0,8},{2,10},{4,12},{6,14},{8,0},{10,2},{12,4},{14,6},{1,9},{3,11}... | collective-permute-start | bytes 196616 | tf_op jit(solution)/shard_map/ppermute | solution.py:25
  71.3 7.8 %collective-permute-start.20 = (bf16[4,16,2048]{2,1,0:T(8,128)(2,1)S(1)}, bf16[4,16,2048]{2,1,0:T(8,128)(2,1)S(1)}, u32[]{:S(2)}, u32[]{:S(2)}) collective-permute-start(bf16[4,16,2048]{2,1,0:T(8,128)(2,1)S(1)} %fusion.16), channel_id=1, source_target_pairs={{0,2},{2,0},{4,6},{6,4},{8,10},{10,8},{12,14},{14,12},{1,3},{3,1},... | collective-permute-start | bytes 786440 | tf_op jit(solution)/shard_map/ppermute | solution.py:25
  72.9 9.8 %collective-permute-start.24 = (bf16[4,16,2048]{2,1,0:T(8,128)(2,1)S(1)}, bf16[4,16,2048]{2,1,0:T(8,128)(2,1)S(1)}, u32[]{:S(2)}, u32[]{:S(2)}) collective-permute-start(bf16[4,16,2048]{2,1,0:T(8,128)(2,1)S(1)} %fusion.17), channel_id=1, source_target_pairs={{0,2},{2,0},{4,6},{6,4},{8,10},{10,8},{12,14},{14,12},{1,3},{3,1},... | collective-permute-start | bytes 786440 | tf_op jit(solution)/shard_map/ppermute | solution.py:25
  79.2 6.5 %collective-permute-start.21 = (bf16[1,16,2048]{2,1,0:T(8,128)(2,1)S(1)}, bf16[1,16,2048]{2,1,0:T(8,128)(2,1)S(1)}, u32[]{:S(2)}, u32[]{:S(2)}) collective-permute-start(bf16[1,16,2048]{2,1,0:T(8,128)(2,1)S(1)} %get-tuple-element.8), channel_id=1, source_target_pairs={{0,4},{2,6},{4,0},{6,2},{8,12},{10,14},{12,8},{14,10},{1,5},{3,7},... | collective-permute-start | bytes 196616 | tf_op jit(solution)/shard_map/ppermute | solution.py:25
  79.3 7.1 %collective-permute-start.23 = (bf16[1,16,2048]{2,1,0:T(8,128)(2,1)S(1)}, bf16[1,16,2048]{2,1,0:T(8,128)(2,1)S(1)}, u32[]{:S(2)}, u32[]{:S(2)}) collective-permute-start(bf16[1,16,2048]{2,1,0:T(8,128)(2,1)S(1)} %get-tuple-element.9), channel_id=1, source_target_pairs={{0,12},{2,14},{4,8},{6,10},{8,4},{10,6},{12,0},{14,2},{1,13},{3,15... | collective-permute-start | bytes 196616 | tf_op jit(solution)/shard_map/ppermute | solution.py:25
  81.1 6.5 %collective-permute-start.22 = (bf16[1,16,2048]{2,1,0:T(8,128)(2,1)S(1)}, bf16[1,16,2048]{2,1,0:T(8,128)(2,1)S(1)}, u32[]{:S(2)}, u32[]{:S(2)}) collective-permute-start(bf16[1,16,2048]{2,1,0:T(8,128)(2,1)S(1)} %get-tuple-element.10), channel_id=1, source_target_pairs={{0,8},{2,10},{4,12},{6,14},{8,0},{10,2},{12,4},{14,6},{1,9},{3,11}... | collective-permute-start | bytes 196616 | tf_op jit(solution)/shard_map/ppermute | solution.py:25
  82.8 4.9 %collective-permute-start.25 = (bf16[1,16,2048]{2,1,0:T(8,128)(2,1)S(1)}, bf16[1,16,2048]{2,1,0:T(8,128)(2,1)S(1)}, u32[]{:S(2)}, u32[]{:S(2)}) collective-permute-start(bf16[1,16,2048]{2,1,0:T(8,128)(2,1)S(1)} %get-tuple-element.11), channel_id=1, source_target_pairs={{0,4},{2,6},{4,0},{6,2},{8,12},{10,14},{12,8},{14,10},{1,5},{3,7},... | collective-permute-start | bytes 196616 | tf_op jit(solution)/shard_map/ppermute | solution.py:25
  83.9 6.1 %collective-permute-start.27 = (bf16[1,16,2048]{2,1,0:T(8,128)(2,1)S(1)}, bf16[1,16,2048]{2,1,0:T(8,128)(2,1)S(1)}, u32[]{:S(2)}, u32[]{:S(2)}) collective-permute-start(bf16[1,16,2048]{2,1,0:T(8,128)(2,1)S(1)} %get-tuple-element.12), channel_id=1, source_target_pairs={{0,12},{2,14},{4,8},{6,10},{8,4},{10,6},{12,0},{14,2},{1,13},{3,15... | collective-permute-start | bytes 196616 | tf_op jit(solution)/shard_map/ppermute | solution.py:25
  85.6 5.7 %collective-permute-start.26 = (bf16[1,16,2048]{2,1,0:T(8,128)(2,1)S(1)}, bf16[1,16,2048]{2,1,0:T(8,128)(2,1)S(1)}, u32[]{:S(2)}, u32[]{:S(2)}) collective-permute-start(bf16[1,16,2048]{2,1,0:T(8,128)(2,1)S(1)} %get-tuple-element.13), channel_id=1, source_target_pairs={{0,8},{2,10},{4,12},{6,14},{8,0},{10,2},{12,4},{14,6},{1,9},{3,11}... | collective-permute-start | bytes 196616 | tf_op jit(solution)/shard_map/ppermute | solution.py:25

commit v5 on v4

--- a/solution.py
+++ b/solution.py
@@ -37,15 +37,33 @@
     return lax.rem(lax.div(lax.axis_index(axis), stride), radix)
 
 
+def groups_of(axis, stride, radix):
+    size = lax.axis_size(axis)
+    return [
+        [i + j * stride for j in range(radix)]
+        for i in range(size)
+        if (i // stride) % radix == 0
+    ]
+
+
 def scatter_level(blocks, axis, stride, radix):
     digit = digit_of(axis, stride, radix)
     view = blocks.reshape((blocks.shape[0] // radix, radix) + blocks.shape[1:])
-    total = lax.dynamic_index_in_dim(view, digit, 1, keepdims=False)
-    for t in range(1, radix):
-        part = lax.dynamic_index_in_dim(view, jnp.bitwise_xor(digit, t), 1, keepdims=False)
-        landed = swap(part.astype(jnp.bfloat16), axis, t * stride)
-        total = total + landed.astype(jnp.float32)
-    return total
+    own = lax.dynamic_index_in_dim(view, digit, 1, keepdims=False)
+    if radix == 2:
+        part = lax.dynamic_index_in_dim(view, 1 - digit, 1, keepdims=False)
+        landed = swap(part.astype(jnp.bfloat16), axis, stride)
+        return own + landed.astype(jnp.float32)
+    landed = lax.all_to_all(
+        view.astype(jnp.bfloat16),
+        axis,
+        1,
+        1,
+        axis_index_groups=groups_of(axis, stride, radix),
+        tiled=True,
+    )
+    kept = own - own.astype(jnp.bfloat16).astype(jnp.float32)
+    return kept + jnp.sum(landed.astype(jnp.float32), axis=1)
 
 
 def scatter_sum(blocks, axis):
@@ -56,13 +74,17 @@
 
 def gather_level(blocks, axis, stride, radix):
     digit = digit_of(axis, stride, radix)
-    held = [blocks] + [swap(blocks, axis, t * stride) for t in range(1, radix)]
-    bit = 1
-    while bit < radix:
-        flip = jnp.bitwise_and(digit, bit) != 0
-        held = [jnp.where(flip, held[j ^ bit], held[j]) for j in range(radix)]
-        bit *= 2
-    whole = jnp.stack(held, axis=1)
+    if radix == 2:
+        other = swap(blocks, axis, stride)
+        pair = [jnp.where(digit == 0, blocks, other), jnp.where(digit == 0, other, blocks)]
+        whole = jnp.stack(pair, axis=1)
+    else:
+        copies = jnp.broadcast_to(
+            blocks[:, None], (blocks.shape[0], radix) + blocks.shape[1:]
+        )
+        whole = lax.all_to_all(
+            copies, axis, 1, 1, axis_index_groups=groups_of(axis, stride, radix), tiled=True
+        )
     return whole.reshape((blocks.shape[0] * radix,) + blocks.shape[1:])
 
 

time: 92.3 us -> 120 us (1.30)
  waiting for transfers between devices: 40.5 us -> 61.5 us
  other arithmetic: 1.44 us -> 4.29 us
  matrix products: 6.68 us -> 8.43 us
  local copies, waits for them, and re-layouts: 1.37 us -> 2.71 us
    all_to_all x0 -> x6, waiting for transfers between devices: none -> 37.4 us  [the longest x4 25.5 us: scatter_level(): lax.all_to_all(view.astype(jnp.bfloat16), axis, 1, 1, axis_index_groups=g...]
    all_to_all x0 -> x6, starting transfers between devices: none -> 25.1 us  [the longest x4 18.3 us: scatter_level(): lax.all_to_all(view.astype(jnp.bfloat16), axis, 1, 1, axis_index_groups=g...]
    ppermute x28 -> x10, starting transfers between devices: 36.7 us -> 12.3 us  [swap(): return lax.ppermute(value, axis, [(i, i ^ distance) for i in range(size)])]
    ppermute x28 -> x10, waiting for transfers between devices: 40.5 us -> 24 us  [swap(): return lax.ppermute(value, axis, [(i, i ^ distance) for i in range(size)])]
    convert_element_type x0 -> x4, other arithmetic: none -> 3.11 us  [scatter_level(): view.astype(jnp.bfloat16)]
    dot_general x2, matrix products: 1.41 us -> 3.16 us  [per_device(): jnp.dot(activations[:, span], chunk.reshape(cols_chunk, width), preferred...]
    broadcast_in_dim x0 -> x2, local copies, waits for them, and re-layouts: none -> 1.47 us  [gather_level(): jnp.broadcast_to(blocks[:, None], (blocks.shape[0], radix) + blocks.shape...]
  transfers between devices with their start and end apart: 28 -> 16, of which waited for: 16 -> 13; matrix products, arithmetic and copies ran while one was open for 4% -> 7% of each run, Pallas kernels for 0% -> 0%
where the time goes in v5:
time: 120 us
  waiting for transfers between devices  61.5 us (51%)
  starting transfers between devices  37.4 us (31%)
  matrix products  8.43 us (7%)
  Pallas kernels  4.43 us (4%)
  other arithmetic  4.29 us (4%)
  local copies, waits for them, and re-layouts  2.71 us (2%)
    all_to_all x4, waiting for transfers between devices, scatter_level(): lax.all_to_all(view.astype(jnp.bfloat16), axis, 1, 1, axis_index_groups=g...  25.5 us
    ppermute x10, waiting for transfers between devices, swap(): return lax.ppermute(value, axis, [(i, i ^ distance) for i in range(size)])  24 us
    all_to_all x4, starting transfers between devices, scatter_level(): lax.all_to_all(view.astype(jnp.bfloat16), axis, 1, 1, axis_index_groups=g...  18.3 us
    ppermute x10, starting transfers between devices, swap(): return lax.ppermute(value, axis, [(i, i ^ distance) for i in range(size)])  12.3 us
    all_to_all x2, waiting for transfers between devices, gather_level(): lax.all_to_all(copies, axis, 1, 1, axis_index_groups=groups_of(axis, stri...  11.9 us
    all_to_all x2, starting transfers between devices, gather_level(): lax.all_to_all(copies, axis, 1, 1, axis_index_groups=groups_of(axis, stri...  6.86 us
    dot_general x2, matrix products, per_device(): lax.dot_general(activations[:, span], start_sketch, (((0,), (0,)), ((), (...  4.66 us
    pallas_call x1, Pallas kernels, make_basis(): pl.pallas_call(functools.partial(basis_kernel, total_cols, root_rows), ou...  4.43 us
  transfers between devices with their start and end apart: 16, of which 13 were waited for; matrix products, arithmetic and copies ran while one was open for 7% of the time, Pallas kernels for 0%

profile of v5, /device:TPU:0, one launch (start us, length us, event | category | flops | bytes accessed | tf_op | source)
XLA Modules:
  0.0 119.5 jit_solution(13423565049404342420)
XLA Ops:
  0.6 0.0 copy-start
  0.7 0.9 copy-done
  1.5 2.3 %fusion.2 = f32[2048,128]{1,0:T(8,128)S(1)} fusion(bf16[512,128]{1,0:T(8,128)(2,1)S(1)} %copy-done, bf16[512,4096]{1,0:T(8,128)(2,1)} %slab_ref.1), kind=kOutput, calls=%fused_computation.2 | convolution fusion | flops 268435456 | bytes 3276800 | tf_op jit(solution)/shard_map/dot_general | solution.py:223
  3.9 3.0 %collective-permute-start.2 = (bf16[4,256,128]{2,1,0:T(8,128)(2,1)S(1)}, bf16[4,256,128]{2,1,0:T(8,128)(2,1)S(1)}, u32[]{:S(2)}, u32[]{:S(2)}) collective-permute-start(bf16[4,256,128]{2,1,0:T(8,128)(2,1)S(1)} %fusion.15), channel_id=1, source_target_pairs={{0,2},{2,0},{4,6},{6,4},{8,10},{10,8},{12,14},{14,12},{1,3},{3,1},... | collective-permute-start | bytes 786440 | tf_op jit(solution)/shard_map/ppermute | solution.py:25
  6.9 2.3 %fusion.6 = f32[2048,128]{1,0:T(8,128)S(1)} fusion(bf16[512,128]{1,0:T(8,128)(2,1)S(1)} %copy-done, bf16[512,4096]{1,0:T(8,128)(2,1)} %slab_ref.1), kind=kOutput, calls=%fused_computation.6 | convolution fusion | flops 268435456 | bytes 3276800 | tf_op jit(solution)/shard_map/dot_general | solution.py:223
  9.3 0.1 collective-permute-start
  9.4 4.7 %collective-permute-done.2 = bf16[4,256,128]{2,1,0:T(8,128)(2,1)S(1)} collective-permute-done((bf16[4,256,128]{2,1,0:T(8,128)(2,1)S(1)}, bf16[4,256,128]{2,1,0:T(8,128)(2,1)S(1)}, u32[]{:S(2)}, u32[]{:S(2)}) %collective-permute-start.2) | collective-permute-done | bytes 262176 | tf_op jit(solution)/shard_map/ppermute | solution.py:25
  14.1 0.8 convert_bitcast_fusion.2
  14.8 5.4 %all-to-all-start.2 = ((bf16[1,4,256,128]{3,2,0,1:T(8,128)(2,1)}), bf16[1,4,256,128]{3,2,0,1:T(8,128)(2,1)S(1)}, u32[]{:S(2)}, u32[]{:S(2)}) async-start(bf16[1,4,256,128]{3,2,0,1:T(8,128)(2,1)} %get-tuple-element.12), calls=%async_computation.2 | async-start | bytes 524288 | tf_op jit(solution)/shard_map/all_to_all | solution.py:57
  20.3 0.8 convert_bitcast_fusion.3
  21.1 6.0 %all-to-all-done.2 = bf16[1,4,256,128]{3,2,0,1:T(8,128)(2,1)S(1)} async-done(((bf16[1,4,256,128]{3,2,0,1:T(8,128)(2,1)}), bf16[1,4,256,128]{3,2,0,1:T(8,128)(2,1)S(1)}, u32[]{:S(2)}, u32[]{:S(2)}) %all-to-all-start.2) | async-done | bytes 262176 | tf_op jit(solution)/shard_map/all_to_all | solution.py:57
  27.1 3.4 %all-to-all-start = ((bf16[1,4,256,128]{3,2,0,1:T(8,128)(2,1)}), bf16[1,4,256,128]{3,2,0,1:T(8,128)(2,1)S(1)}, u32[]{:S(2)}, u32[]{:S(2)}) async-start(bf16[1,4,256,128]{3,2,0,1:T(8,128)(2,1)} %get-tuple-element.10), calls=%async_computation | async-start | bytes 524288 | tf_op jit(solution)/shard_map/all_to_all | solution.py:57
  30.6 6.7 %all-to-all-done = bf16[1,4,256,128]{3,2,0,1:T(8,128)(2,1)S(1)} async-done(((bf16[1,4,256,128]{3,2,0,1:T(8,128)(2,1)}), bf16[1,4,256,128]{3,2,0,1:T(8,128)(2,1)S(1)}, u32[]{:S(2)}, u32[]{:S(2)}) %all-to-all-start) | async-done | bytes 262176 | tf_op jit(solution)/shard_map/all_to_all | solution.py:57
  37.3 0.7 broadcast_in_dim.5
  38.0 3.4 %all-to-all-start.3 = ((bf16[1,4,256,128]{3,2,0,1:T(8,128)(2,1)}), bf16[1,4,256,128]{3,2,0,1:T(8,128)(2,1)S(1)}, u32[]{:S(2)}, u32[]{:S(2)}) async-start(bf16[1,4,256,128]{3,2,0,1:T(8,128)(2,1)} %broadcast_in_dim.5), calls=%async_computation.3 | async-start | bytes 524288 | tf_op jit(solution)/shard_map/all_to_all | solution.py:85
  41.5 6.7 %all-to-all-done.3 = bf16[1,4,256,128]{3,2,0,1:T(8,128)(2,1)S(1)} async-done(((bf16[1,4,256,128]{3,2,0,1:T(8,128)(2,1)}), bf16[1,4,256,128]{3,2,0,1:T(8,128)(2,1)S(1)}, u32[]{:S(2)}, u32[]{:S(2)}) %all-to-all-start.3) | async-done | bytes 262176 | tf_op jit(solution)/shard_map/all_to_all | solution.py:85
  48.2 0.7 broadcast_in_dim.4
  48.9 3.4 %all-to-all-start.1 = ((bf16[1,4,256,128]{3,2,0,1:T(8,128)(2,1)}), bf16[1,4,256,128]{3,2,0,1:T(8,128)(2,1)S(1)}, u32[]{:S(2)}, u32[]{:S(2)}) async-start(bf16[1,4,256,128]{3,2,0,1:T(8,128)(2,1)} %broadcast_in_dim.4), calls=%async_computation.1 | async-start | bytes 524288 | tf_op jit(solution)/shard_map/all_to_all | solution.py:85
  52.4 1.5 %collective-permute-start.3 = (bf16[4,256,128]{2,1,0:T(8,128)(2,1)S(1)}, bf16[4,256,128]{2,1,0:T(8,128)(2,1)S(1)}, u32[]{:S(2)}, u32[]{:S(2)}) collective-permute-start(bf16[4,256,128]{2,1,0:T(8,128)(2,1)S(1)} %bitcast.116), channel_id=1, source_target_pairs={{0,2},{2,0},{4,6},{6,4},{8,10},{10,8},{12,14},{14,12},{1,3},{3,1},... | collective-permute-start | bytes 786440 | tf_op jit(solution)/shard_map/ppermute | solution.py:25
  53.9 5.2 %all-to-all-done.1 = bf16[1,4,256,128]{3,2,0,1:T(8,128)(2,1)S(1)} async-done(((bf16[1,4,256,128]{3,2,0,1:T(8,128)(2,1)}), bf16[1,4,256,128]{3,2,0,1:T(8,128)(2,1)S(1)}, u32[]{:S(2)}, u32[]{:S(2)}) %all-to-all-start.1) | async-done | bytes 262176 | tf_op jit(solution)/shard_map/all_to_all | solution.py:85
  59.2 1.5 %collective-permute-start.1 = (bf16[4,256,128]{2,1,0:T(8,128)(2,1)S(1)}, bf16[4,256,128]{2,1,0:T(8,128)(2,1)S(1)}, u32[]{:S(2)}, u32[]{:S(2)}) collective-permute-start(bf16[4,256,128]{2,1,0:T(8,128)(2,1)S(1)} %bitcast.117), channel_id=1, source_target_pairs={{0,2},{2,0},{4,6},{6,4},{8,10},{10,8},{12,14},{14,12},{1,3},{3,1},... | collective-permute-start | bytes 786440 | tf_op jit(solution)/shard_map/ppermute | solution.py:25
  60.7 0.1 pad_maximum_fusion.1
  60.8 0.0 copy-start.1
  60.8 2.5 %fusion = f32[128,512]{0,1:T(8,128)S(1)} fusion(bf16[2048,128]{1,0:T(8,128)(2,1)S(1)} %bitcast.123, bf16[512,4096]{1,0:T(8,128)(2,1)} %slab_ref.1), kind=kOutput, calls=%fused_computation | convolution fusion | flops 268435456 | bytes 2883584 | tf_op jit(solution)/shard_map/dot_general | solution.py:231
  63.3 2.3 %collective-permute-done.1 = bf16[4,256,128]{2,1,0:T(8,128)(2,1)S(1)} collective-permute-done((bf16[4,256,128]{2,1,0:T(8,128)(2,1)S(1)}, bf16[4,256,128]{2,1,0:T(8,128)(2,1)S(1)}, u32[]{:S(2)}, u32[]{:S(2)}) %collective-permute-start.1) | collective-permute-done | bytes 262176 | tf_op jit(solution)/shard_map/ppermute | solution.py:25
  65.6 0.1 pad_maximum_fusion
  65.6 0.7 fusion.11.mine_ref
  66.4 0.1 collective-permute-start.4
  66.4 1.5 %collective-permute-done.4.other_ref = f32[512,128]{1,0:T(8,128)S(1)} collective-permute-done((f32[512,128]{1,0:T(8,128)S(1)}, f32[512,128]{1,0:T(8,128)S(1)}, u32[]{:S(2)}, u32[]{:S(2)}) %collective-permute-start.4) | collective-permute-done | bytes 262176 | tf_op jit(solution)/shard_map/ppermute | solution.py:25
  68.0 0.6 fusion.18
  68.6 1.6 %collective-permute-start.5 = (f32[128,128]{1,0:T(8,128)S(1)}, f32[128,128]{1,0:T(8,128)S(1)}, u32[]{:S(2)}, u32[]{:S(2)}) collective-permute-start(f32[128,128]{1,0:T(8,128)S(1)} %fusion.18), channel_id=1, source_target_pairs={{0,2},{2,0},{4,6},{6,4},{8,10},{10,8},{12,14},{14,12},{1,3},{3,1},... | collective-permute-start | bytes 196616 | tf_op jit(solution)/shard_map/ppermute | solution.py:25
  70.1 2.8 %collective-permute-done.5 = f32[128,128]{1,0:T(8,128)S(1)} collective-permute-done((f32[128,128]{1,0:T(8,128)S(1)}, f32[128,128]{1,0:T(8,128)S(1)}, u32[]{:S(2)}, u32[]{:S(2)}) %collective-permute-start.5) | collective-permute-done | bytes 65568 | tf_op jit(solution)/shard_map/ppermute | solution.py:25
  72.9 1.5 %collective-permute-start.6 = (f32[128,128]{1,0:T(8,128)S(1)}, f32[128,128]{1,0:T(8,128)S(1)}, u32[]{:S(2)}, u32[]{:S(2)}) collective-permute-start(f32[128,128]{1,0:T(8,128)S(1)} %add.74), channel_id=1, source_target_pairs={{0,4},{2,6},{4,0},{6,2},{8,12},{10,14},{12,8},{14,10},{1,5},{3,7},... | collective-permute-start | bytes 196616 | tf_op jit(solution)/shard_map/ppermute | solution.py:25
  74.4 2.8 %collective-permute-done.6 = f32[128,128]{1,0:T(8,128)S(1)} collective-permute-done((f32[128,128]{1,0:T(8,128)S(1)}, f32[128,128]{1,0:T(8,128)S(1)}, u32[]{:S(2)}, u32[]{:S(2)}) %collective-permute-start.6) | collective-permute-done | bytes 65568 | tf_op jit(solution)/shard_map/ppermute | solution.py:25
  77.3 0.8 collective-permute-start.7
  78.1 4.4 %collective-permute-done.7 = f32[128,128]{1,0:T(8,128)S(1)} collective-permute-done((f32[128,128]{1,0:T(8,128)S(1)}, f32[128,128]{1,0:T(8,128)S(1)}, u32[]{:S(2)}, u32[]{:S(2)}) %collective-permute-start.7) | collective-permute-done | bytes 65568 | tf_op jit(solution)/shard_map/ppermute | solution.py:25
  82.5 4.4 %make_basis.1 = (f32[512,128]{1,0:T(8,128)}, f32[128,4096]{1,0:T(8,128)S(1)}) custom-call(f32[128,128]{1,0:T(8,128)S(1)} %add.76.gram_ref, f32[512,128]{1,0:T(8,128)S(1)} %fusion.11.mine_ref, f32[512,128]{1,0:T(8,128)S(1)} %collective-permute-done.4.other_ref, bf16[512,4096]{1,0:T(8,128)(2,1)S(1)} %copy-done.1), custom_call_target="tpu_custom_call" | custom-call | tf_op jit(solution)/shard_map/make_basis/pallas_call | solution.py:193
  86.9 0.1 fusion.33
  87.1 1.6 %collective-permute-start.8 = (bf16[4,16,2048]{2,1,0:T(8,128)(2,1)S(1)}, bf16[4,16,2048]{2,1,0:T(8,128)(2,1)S(1)}, u32[]{:S(2)}, u32[]{:S(2)}) collective-permute-start(bf16[4,16,2048]{2,1,0:T(8,128)(2,1)S(1)} %fusion.16), channel_id=1, source_target_pairs={{0,2},{2,0},{4,6},{6,4},{8,10},{10,8},{12,14},{14,12},{1,3},{3,1},... | collective-permute-start | bytes 786440 | tf_op jit(solution)/shard_map/ppermute | solution.py:25
  88.7 0.6 collective-permute-start.9
  89.3 5.6 %collective-permute-done.8 = bf16[4,16,2048]{2,1,0:T(8,128)(2,1)S(1)} collective-permute-done((bf16[4,16,2048]{2,1,0:T(8,128)(2,1)S(1)}, bf16[4,16,2048]{2,1,0:T(8,128)(2,1)S(1)}, u32[]{:S(2)}, u32[]{:S(2)}) %collective-permute-start.8) | collective-permute-done | bytes 262176 | tf_op jit(solution)/shard_map/ppermute | solution.py:25
  94.9 0.8 convert_bitcast_fusion.1
  95.7 3.9 %all-to-all-start.4 = ((bf16[1,4,16,2048]{3,2,0,1:T(8,128)(2,1)}), bf16[1,4,16,2048]{3,2,0,1:T(8,128)(2,1)S(1)}, u32[]{:S(2)}, u32[]{:S(2)}) async-start(bf16[1,4,16,2048]{3,2,0,1:T(8,128)(2,1)} %get-tuple-element.6), calls=%async_computation.4 | async-start | bytes 524288 | tf_op jit(solution)/shard_map/all_to_all | solution.py:57
  99.6 0.8 convert_bitcast_fusion
  100.3 6.1 %all-to-all-done.4 = bf16[1,4,16,2048]{3,2,0,1:T(8,128)(2,1)S(1)} async-done(((bf16[1,4,16,2048]{3,2,0,1:T(8,128)(2,1)}), bf16[1,4,16,2048]{3,2,0,1:T(8,128)(2,1)S(1)}, u32[]{:S(2)}, u32[]{:S(2)}) %all-to-all-start.4) | async-done | bytes 262176 | tf_op jit(solution)/shard_map/all_to_all | solution.py:57
  106.4 5.5 %all-to-all-start.5 = ((bf16[1,4,16,2048]{3,2,0,1:T(8,128)(2,1)}), bf16[1,4,16,2048]{3,2,0,1:T(8,128)(2,1)S(1)}, u32[]{:S(2)}, u32[]{:S(2)}) async-start(bf16[1,4,16,2048]{3,2,0,1:T(8,128)(2,1)} %get-tuple-element.8), calls=%async_computation.5 | async-start | bytes 524288 | tf_op jit(solution)/shard_map/all_to_all | solution.py:57
  112.0 6.7 %all-to-all-done.5 = bf16[1,4,16,2048]{3,2,0,1:T(8,128)(2,1)S(1)} async-done(((bf16[1,4,16,2048]{3,2,0,1:T(8,128)(2,1)}), bf16[1,4,16,2048]{3,2,0,1:T(8,128)(2,1)S(1)}, u32[]{:S(2)}, u32[]{:S(2)}) %all-to-all-start.5) | async-done | bytes 262176 | tf_op jit(solution)/shard_map/all_to_all | solution.py:57
  118.8 0.7 pad_maximum_fusion.2
  (22 shorter events, 0.6 us)
Async XLA Ops:
  0.6 0.9 copy-start
  3.9 10.1 %collective-permute-start.2 = (bf16[4,256,128]{2,1,0:T(8,128)(2,1)S(1)}, bf16[4,256,128]{2,1,0:T(8,128)(2,1)S(1)}, u32[]{:S(2)}, u32[]{:S(2)}) collective-permute-start(bf16[4,256,128]{2,1,0:T(8,128)(2,1)S(1)} %fusion.15), channel_id=1, source_target_pairs={{0,2},{2,0},{4,6},{6,4},{8,10},{10,8},{12,14},{14,12},{1,3},{3,1},... | collective-permute-start | bytes 786440 | tf_op jit(solution)/shard_map/ppermute | solution.py:25
  9.3 11.0 %collective-permute-start = (bf16[4,256,128]{2,1,0:T(8,128)(2,1)S(1)}, bf16[4,256,128]{2,1,0:T(8,128)(2,1)S(1)}, u32[]{:S(2)}, u32[]{:S(2)}) collective-permute-start(bf16[4,256,128]{2,1,0:T(8,128)(2,1)S(1)} %fusion.14), channel_id=1, source_target_pairs={{0,2},{2,0},{4,6},{6,4},{8,10},{10,8},{12,14},{14,12},{1,3},{3,1},... | collective-permute-start | bytes 786440 | tf_op jit(solution)/shard_map/ppermute | solution.py:25
  14.8 12.2 %all-to-all-start.2 = ((bf16[1,4,256,128]{3,2,0,1:T(8,128)(2,1)}), bf16[1,4,256,128]{3,2,0,1:T(8,128)(2,1)S(1)}, u32[]{:S(2)}, u32[]{:S(2)}) async-start(bf16[1,4,256,128]{3,2,0,1:T(8,128)(2,1)} %get-tuple-element.12), calls=%async_computation.2 | async-start | bytes 524288 | tf_op jit(solution)/shard_map/all_to_all | solution.py:57
  27.1 10.2 %all-to-all-start = ((bf16[1,4,256,128]{3,2,0,1:T(8,128)(2,1)}), bf16[1,4,256,128]{3,2,0,1:T(8,128)(2,1)S(1)}, u32[]{:S(2)}, u32[]{:S(2)}) async-start(bf16[1,4,256,128]{3,2,0,1:T(8,128)(2,1)} %get-tuple-element.10), calls=%async_computation | async-start | bytes 524288 | tf_op jit(solution)/shard_map/all_to_all | solution.py:57
  38.0 10.2 %all-to-all-start.3 = ((bf16[1,4,256,128]{3,2,0,1:T(8,128)(2,1)}), bf16[1,4,256,128]{3,2,0,1:T(8,128)(2,1)S(1)}, u32[]{:S(2)}, u32[]{:S(2)}) async-start(bf16[1,4,256,128]{3,2,0,1:T(8,128)(2,1)} %broadcast_in_dim.5), calls=%async_computation.3 | async-start | bytes 524288 | tf_op jit(solution)/shard_map/all_to_all | solution.py:85
  48.9 10.2 %all-to-all-start.1 = ((bf16[1,4,256,128]{3,2,0,1:T(8,128)(2,1)}), bf16[1,4,256,128]{3,2,0,1:T(8,128)(2,1)S(1)}, u32[]{:S(2)}, u32[]{:S(2)}) async-start(bf16[1,4,256,128]{3,2,0,1:T(8,128)(2,1)} %broadcast_in_dim.4), calls=%async_computation.1 | async-start | bytes 524288 | tf_op jit(solution)/shard_map/all_to_all | solution.py:85
  52.4 8.3 %collective-permute-start.3 = (bf16[4,256,128]{2,1,0:T(8,128)(2,1)S(1)}, bf16[4,256,128]{2,1,0:T(8,128)(2,1)S(1)}, u32[]{:S(2)}, u32[]{:S(2)}) collective-permute-start(bf16[4,256,128]{2,1,0:T(8,128)(2,1)S(1)} %bitcast.116), channel_id=1, source_target_pairs={{0,2},{2,0},{4,6},{6,4},{8,10},{10,8},{12,14},{14,12},{1,3},{3,1},... | collective-permute-start | bytes 786440 | tf_op jit(solution)/shard_map/ppermute | solution.py:25
  59.2 6.4 %collective-permute-start.1 = (bf16[4,256,128]{2,1,0:T(8,128)(2,1)S(1)}, bf16[4,256,128]{2,1,0:T(8,128)(2,1)S(1)}, u32[]{:S(2)}, u32[]{:S(2)}) collective-permute-start(bf16[4,256,128]{2,1,0:T(8,128)(2,1)S(1)} %bitcast.117), channel_id=1, source_target_pairs={{0,2},{2,0},{4,6},{6,4},{8,10},{10,8},{12,14},{14,12},{1,3},{3,1},... | collective-permute-start | bytes 786440 | tf_op jit(solution)/shard_map/ppermute | solution.py:25
  60.8 4.8 %copy-start.1 = (bf16[512,4096]{1,0:T(8,128)(2,1)S(1)}, bf16[512,4096]{1,0:T(8,128)(2,1)}, u32[]{:S(2)}) copy-start(bf16[512,4096]{1,0:T(8,128)(2,1)} %slab_ref.1) | copy-start | bytes 12582916
  66.4 1.6 %collective-permute-start.4 = (f32[512,128]{1,0:T(8,128)S(1)}, f32[512,128]{1,0:T(8,128)S(1)}, u32[]{:S(2)}, u32[]{:S(2)}) collective-permute-start(f32[512,128]{1,0:T(8,128)S(1)} %fusion.11.mine_ref), channel_id=1, source_target_pairs={{0,1},{1,0},{2,3},{3,2},{4,5},{5,4},{6,7},{7,6},{8,9},{9,8},{10,11... | collective-permute-start | bytes 786440 | tf_op jit(solution)/shard_map/ppermute | solution.py:25
  68.6 4.3 %collective-permute-start.5 = (f32[128,128]{1,0:T(8,128)S(1)}, f32[128,128]{1,0:T(8,128)S(1)}, u32[]{:S(2)}, u32[]{:S(2)}) collective-permute-start(f32[128,128]{1,0:T(8,128)S(1)} %fusion.18), channel_id=1, source_target_pairs={{0,2},{2,0},{4,6},{6,4},{8,10},{10,8},{12,14},{14,12},{1,3},{3,1},... | collective-permute-start | bytes 196616 | tf_op jit(solution)/shard_map/ppermute | solution.py:25
  72.9 4.3 %collective-permute-start.6 = (f32[128,128]{1,0:T(8,128)S(1)}, f32[128,128]{1,0:T(8,128)S(1)}, u32[]{:S(2)}, u32[]{:S(2)}) collective-permute-start(f32[128,128]{1,0:T(8,128)S(1)} %add.74), channel_id=1, source_target_pairs={{0,4},{2,6},{4,0},{6,2},{8,12},{10,14},{12,8},{14,10},{1,5},{3,7},... | collective-permute-start | bytes 196616 | tf_op jit(solution)/shard_map/ppermute | solution.py:25
  77.3 5.2 %collective-permute-start.7 = (f32[128,128]{1,0:T(8,128)S(1)}, f32[128,128]{1,0:T(8,128)S(1)}, u32[]{:S(2)}, u32[]{:S(2)}) collective-permute-start(f32[128,128]{1,0:T(8,128)S(1)} %add.75), channel_id=1, source_target_pairs={{0,8},{2,10},{4,12},{6,14},{8,0},{10,2},{12,4},{14,6},{1,9},{3,11}... | collective-permute-start | bytes 196616 | tf_op jit(solution)/shard_map/ppermute | solution.py:25
  87.1 7.8 %collective-permute-start.8 = (bf16[4,16,2048]{2,1,0:T(8,128)(2,1)S(1)}, bf16[4,16,2048]{2,1,0:T(8,128)(2,1)S(1)}, u32[]{:S(2)}, u32[]{:S(2)}) collective-permute-start(bf16[4,16,2048]{2,1,0:T(8,128)(2,1)S(1)} %fusion.16), channel_id=1, source_target_pairs={{0,2},{2,0},{4,6},{6,4},{8,10},{10,8},{12,14},{14,12},{1,3},{3,1},... | collective-permute-start | bytes 786440 | tf_op jit(solution)/shard_map/ppermute | solution.py:25
  88.7 10.8 %collective-permute-start.9 = (bf16[4,16,2048]{2,1,0:T(8,128)(2,1)S(1)}, bf16[4,16,2048]{2,1,0:T(8,128)(2,1)S(1)}, u32[]{:S(2)}, u32[]{:S(2)}) collective-permute-start(bf16[4,16,2048]{2,1,0:T(8,128)(2,1)S(1)} %fusion.17), channel_id=1, source_target_pairs={{0,2},{2,0},{4,6},{6,4},{8,10},{10,8},{12,14},{14,12},{1,3},{3,1},... | collective-permute-start | bytes 786440 | tf_op jit(solution)/shard_map/ppermute | solution.py:25
  95.7 10.7 %all-to-all-start.4 = ((bf16[1,4,16,2048]{3,2,0,1:T(8,128)(2,1)}), bf16[1,4,16,2048]{3,2,0,1:T(8,128)(2,1)S(1)}, u32[]{:S(2)}, u32[]{:S(2)}) async-start(bf16[1,4,16,2048]{3,2,0,1:T(8,128)(2,1)} %get-tuple-element.6), calls=%async_computation.4 | async-start | bytes 524288 | tf_op jit(solution)/shard_map/all_to_all | solution.py:57
  106.4 12.3 %all-to-all-start.5 = ((bf16[1,4,16,2048]{3,2,0,1:T(8,128)(2,1)}), bf16[1,4,16,2048]{3,2,0,1:T(8,128)(2,1)S(1)}, u32[]{:S(2)}, u32[]{:S(2)}) async-start(bf16[1,4,16,2048]{3,2,0,1:T(8,128)(2,1)} %get-tuple-element.8), calls=%async_computation.5 | async-start | bytes 524288 | tf_op jit(solution)/shard_map/all_to_all | solution.py:57

commit v6 on v4

--- a/solution.py
+++ b/solution.py
@@ -54,23 +54,84 @@
     return blocks[0]
 
 
-def gather_level(blocks, axis, stride, radix):
-    digit = digit_of(axis, stride, radix)
-    held = [blocks] + [swap(blocks, axis, t * stride) for t in range(1, radix)]
-    bit = 1
-    while bit < radix:
-        flip = jnp.bitwise_and(digit, bit) != 0
-        held = [jnp.where(flip, held[j ^ bit], held[j]) for j in range(radix)]
-        bit *= 2
-    whole = jnp.stack(held, axis=1)
-    return whole.reshape((blocks.shape[0] * radix,) + blocks.shape[1:])
-
-
-def gather(block, axis):
-    blocks = block[None]
-    for stride, radix in reversed(levels_of(lax.axis_size(axis))):
-        blocks = gather_level(blocks, axis, stride, radix)
-    return blocks
+def bit_of(axis, bit):
+    return lax.rem(lax.div(lax.axis_index(axis), 1 << bit), 2)
+
+
+def halve(value, upper):
+    width = value.shape[1] // 2
+    low, high = value[:, :width], value[:, width:]
+    return jnp.where(upper, high, low), jnp.where(upper, low, high)
+
+
+def sum_and_share(keep, send, axis, scale):
+    bits = (lax.axis_size(axis) - 1).bit_length()
+    total = keep + swap(send, axis, 1).astype(jnp.float32)
+    for bit in range(1, bits - 1):
+        keep, send = halve(total, bit_of(axis, bit) == 1)
+        total = keep + swap(send.astype(jnp.bfloat16), axis, 1 << bit).astype(jnp.float32)
+    other = swap(total.astype(jnp.bfloat16), axis, 1 << (bits - 1))
+    block = ((total + other.astype(jnp.float32)) * scale).astype(jnp.bfloat16)
+    for bit in reversed(range(bits - 1)):
+        other = swap(block, axis, 1 << bit)
+        upper = bit_of(axis, bit) == 1
+        block = jnp.concatenate(
+            [jnp.where(upper, other, block), jnp.where(upper, block, other)], axis=1
+        )
+    return block
+
+
+def sketch_kernel(plan, half, sketch_ref, slab_ref, *refs):
+    outs, buffers, arrived = refs[-2 - len(plan) : -2], refs[-2], refs[-1]
+    digit = bit_of("row", 0)
+    jobs = []
+    for out, (first, sent) in enumerate(plan):
+        begin = (first + (1 - digit if sent else digit)) * half
+        for tile in range(half // SKETCH_TILE):
+            here = pl.multiple_of(begin + tile * SKETCH_TILE, SKETCH_TILE)
+            slot = len(jobs)
+            copy = pltpu.make_async_copy(
+                slab_ref.at[:, pl.ds(here, SKETCH_TILE)], buffers.at[slot], arrived.at[slot]
+            )
+            copy.start()
+            jobs.append((out, tile, copy))
+    left = sketch_ref[...].T
+    for slot, (out, tile, copy) in enumerate(jobs):
+        copy.wait()
+        product = lax.dot_general(
+            left, buffers[slot], (((1,), (0,)), ((), ())), preferred_element_type=jnp.float32
+        )
+        span = slice(tile * SKETCH_TILE, (tile + 1) * SKETCH_TILE)
+        outs[out][:, span] = product.astype(outs[out].dtype)
+
+
+def sketch_halves(slab, start, plan, half, after=()):
+    rows, width = start.shape
+    tiles = len(plan) * (half // SKETCH_TILE)
+    return pl.pallas_call(
+        functools.partial(sketch_kernel, plan, half),
+        out_shape=[
+            jax.ShapeDtypeStruct((width, half), jnp.bfloat16 if sent else jnp.float32)
+            for _, sent in plan
+        ],
+        in_specs=[
+            pl.BlockSpec(memory_space=pltpu.VMEM),
+            pl.BlockSpec(memory_space=pl.ANY),
+        ]
+        + [pl.BlockSpec(memory_space=pl.ANY)] * len(after),
+        out_specs=[pl.BlockSpec(memory_space=pltpu.VMEM)] * len(plan),
+        scratch_shapes=[
+            pltpu.VMEM((tiles, rows, SKETCH_TILE), jnp.bfloat16),
+            pltpu.SemaphoreType.DMA((tiles,)),
+        ],
+        compiler_params=pltpu.CompilerParams(vmem_limit_bytes=57 * 2**20),
+        cost_estimate=pl.CostEstimate(
+            flops=2 * rows * width * half * len(plan),
+            bytes_accessed=2 * rows * half * len(plan),
+            transcendentals=0,
+        ),
+        name="sketch_halves",
+    )(start, slab, *after)
 
 
 def matmul(left, right, exact=True):
@@ -101,6 +162,7 @@
 LOOSE_UPDATES = 2
 CLOSE = 1e-5
 TILE = 1024
+SKETCH_TILE = 512
 
 
 def basis_kernel(
@@ -196,19 +258,23 @@
     cols_chunk = cols_here // CHUNKS
     spans = [slice(c * cols_chunk, (c + 1) * cols_chunk) for c in range(CHUNKS)]
 
+    half = cols_chunk // 2
+    (send,) = sketch_halves(activations, start_sketch, [(0, True)], half)
+    sends, keeps = [send], []
+    plan = [(0, False)]
+    for c in range(1, CHUNKS):
+        plan += [(2 * c, True), (2 * c, False)]
+    rest = sketch_halves(activations, start_sketch, plan, half, (send,))
+    for (_, sent), out in zip(plan, rest):
+        (sends if sent else keeps).append(out)
+
     partial_sketch = 0.0
-    for span in spans:
-        local_cols = lax.dot_general(
+    for span, keep, send in zip(spans, keeps, sends):
+        shared = sum_and_share(keep, send, "row", 1.0 / root_rows)
+        partial_sketch = partial_sketch + lax.dot_general(
             activations[:, span],
-            start_sketch,
-            (((0,), (0,)), ((), ())),
-            preferred_element_type=jnp.float32,
-        )
-        share = scatter_sum(local_cols.reshape(parts, cols_chunk // parts, width), "row")
-        chunk = gather((share / root_rows).astype(jnp.bfloat16), "row")
-        partial_sketch = partial_sketch + jnp.dot(
-            activations[:, span],
-            chunk.reshape(cols_chunk, width),
+            shared,
+            (((1,), (1,)), ((), ())),
             preferred_element_type=jnp.float32,
         )
     other_sketch = swap(partial_sketch, "col", 1)

time: 92.3 us -> 99.8 us (1.081)
  Pallas kernels: 4.43 us -> 11.9 us
  waiting for transfers between devices: 40.5 us -> 47.3 us
  matrix products: 6.68 us -> 2.05 us
  starting transfers between devices: 36.7 us -> 32.2 us
  other arithmetic: 1.44 us -> 2.72 us
  local copies, waits for them, and re-layouts: 1.37 us -> 2.47 us
    pallas_call x0 -> x2, Pallas kernels: none -> 7.45 us  [sketch_halves(): pl.pallas_call(functools.partial(sketch_kernel, plan, half), out_shape=[j...]
    ppermute x28 -> x22, waiting for transfers between devices: 40.5 us -> 47.3 us  [swap(): return lax.ppermute(value, axis, [(i, i ^ distance) for i in range(size)])]
    dot_general x4 -> x2, matrix products: 6.07 us -> 1.44 us  [per_device(): lax.dot_general(activations[:, span], shared, (((1,), (1,)), ((), ())), p...]
    ppermute x28 -> x22, starting transfers between devices: 36.7 us -> 32.2 us  [swap(): return lax.ppermute(value, axis, [(i, i ^ distance) for i in range(size)])]
    unnamed x4 -> x8, local copies, waits for them, and re-layouts: 0.9 us -> 2.2 us
    add x0 -> x2, other arithmetic: none -> 1.15 us  [sum_and_share(): total = keep + swap(send, axis, 1).astype(jnp.float32)]
  transfers between devices with their start and end apart: 28 -> 22, of which waited for: 16 -> 15; matrix products, arithmetic and copies ran while one was open for 4% -> 3% of each run, Pallas kernels for 0% -> 0%
where the time goes in v6:
time: 99.8 us; the launch traced here: 99.5 us
  waiting for transfers between devices  47.3 us (47%)
  starting transfers between devices  32.2 us (32%)
  Pallas kernels  11.9 us (12%)
  other arithmetic  2.72 us (3%)
  local copies, waits for them, and re-layouts  2.47 us (2%)
  matrix products  2.05 us (2%)
    ppermute x22, waiting for transfers between devices, swap(): return lax.ppermute(value, axis, [(i, i ^ distance) for i in range(size)])  47.3 us
    ppermute x22, starting transfers between devices, swap(): return lax.ppermute(value, axis, [(i, i ^ distance) for i in range(size)])  32.2 us
    pallas_call x2, Pallas kernels, sketch_halves(): pl.pallas_call(functools.partial(sketch_kernel, plan, half), out_shape=[j...  7.45 us
    pallas_call x1, Pallas kernels, make_basis(): pl.pallas_call(functools.partial(basis_kernel, total_cols, root_rows), ou...  4.43 us
    unnamed x8, local copies, waits for them, and re-layouts  2.2 us
  transfers between devices with their start and end apart: 22, of which 15 were waited for; matrix products, arithmetic and copies ran while one was open for 3% of the time, Pallas kernels for 0%

profile of v6, /device:TPU:0, one launch (start us, length us, event | category | flops | bytes accessed | tf_op | source)
XLA Modules:
  0.0 99.5 jit_solution(10323580226587198808)
XLA Ops:
  0.6 3.1 %sketch_halves.2.refs_0_ = bf16[128,1024]{1,0:T(8,128)(2,1)} custom-call(bf16[512,128]{1,0:T(8,128)(2,1)} %sketch_ref.3, bf16[512,4096]{1,0:T(8,128)(2,1)} %slab_ref.5), custom_call_target="tpu_custom_call" | custom-call | flops 134217728 | bytes 1048576 | tf_op jit(solution)/shard_map/sketch_halves/pallas_call | solution.py:111
  3.8 4.3 %sketch_halves.3 = (f32[128,1024]{1,0:T(8,128)}, bf16[128,1024]{1,0:T(8,128)(2,1)}, f32[128,1024]{1,0:T(8,128)}) custom-call(bf16[512,128]{1,0:T(8,128)(2,1)} %sketch_ref.3, bf16[512,4096]{1,0:T(8,128)(2,1)} %slab_ref.5, bf16[128,1024]{1,0:T(8,128)(2,1)} %sketch_halves.2.refs_0_), custom_call_target="tpu_custom_call" | custom-call | flops 402653184 | bytes 3145728 | tf_op jit(solution)/shard_map/sketch_halves/pallas_call | solution.py:111
  8.1 3.0 %collective-permute-start.5 = (bf16[128,1024]{1,0:T(8,128)(2,1)}, bf16[128,1024]{1,0:T(8,128)(2,1)S(1)}, u32[]{:S(2)}, u32[]{:S(2)}) collective-permute-start(bf16[128,1024]{1,0:T(8,128)(2,1)} %get-tuple-element.9), channel_id=1, source_target_pairs={{0,2},{2,0},{4,6},{6,4},{8,10},{10,8},{12,14},{14,12},{1,3},{3,1},... | collective-permute-start | bytes 786440 | tf_op jit(solution)/shard_map/ppermute | solution.py:25
  11.1 0.1 collective-permute-start
  11.2 7.3 %collective-permute-done.5 = bf16[128,1024]{1,0:T(8,128)(2,1)S(1)} collective-permute-done((bf16[128,1024]{1,0:T(8,128)(2,1)}, bf16[128,1024]{1,0:T(8,128)(2,1)S(1)}, u32[]{:S(2)}, u32[]{:S(2)}) %collective-permute-start.5) | collective-permute-done | bytes 262176 | tf_op jit(solution)/shard_map/ppermute | solution.py:25
  18.5 1.1 %convert_add_fusion = f32[128,1024]{1,0:T(8,128)S(1)} fusion(f32[128,1024]{1,0:T(8,128)} %get-tuple-element.8, bf16[128,1024]{1,0:T(8,128)(2,1)S(1)} %collective-permute-done.5), kind=kLoop, calls=%fused_computation.16 | loop fusion | flops 262144 | bytes 1310720 | tf_op jit(solution)/shard_map/add | solution.py:69
  19.6 2.2 %collective-permute-start.6 = (bf16[128,512]{1,0:T(8,128)(2,1)S(1)}, bf16[128,512]{1,0:T(8,128)(2,1)S(1)}, u32[]{:S(2)}, u32[]{:S(2)}) collective-permute-start(bf16[128,512]{1,0:T(8,128)(2,1)S(1)} %select_convert_fusion), channel_id=1, source_target_pairs={{0,4},{2,6},{4,0},{6,2},{8,12},{10,14},{12,8},{14,10},{1,5},{3,7},... | collective-permute-start | bytes 393224 | tf_op jit(solution)/shard_map/ppermute | solution.py:25
  21.8 1.4 %collective-permute-done = bf16[128,1024]{1,0:T(8,128)(2,1)S(1)} collective-permute-done((bf16[128,1024]{1,0:T(8,128)(2,1)S(1)}, bf16[128,1024]{1,0:T(8,128)(2,1)S(1)}, u32[]{:S(2)}, u32[]{:S(2)}) %collective-permute-start) | collective-permute-done | bytes 262176 | tf_op jit(solution)/shard_map/ppermute | solution.py:25
  23.4 1.9 %collective-permute-start.1 = (bf16[128,512]{1,0:T(8,128)(2,1)S(1)}, bf16[128,512]{1,0:T(8,128)(2,1)S(1)}, u32[]{:S(2)}, u32[]{:S(2)}) collective-permute-start(bf16[128,512]{1,0:T(8,128)(2,1)S(1)} %select_convert_fusion.1), channel_id=1, source_target_pairs={{0,4},{2,6},{4,0},{6,2},{8,12},{10,14},{12,8},{14,10},{1,5},{3,7},... | collective-permute-start | bytes 393224 | tf_op jit(solution)/shard_map/ppermute | solution.py:25
  25.3 2.7 %collective-permute-start.7 = (bf16[128,512]{1,0:T(8,128)(2,1)S(1)}, bf16[128,512]{1,0:T(8,128)(2,1)S(1)}, u32[]{:S(2)}, u32[]{:S(2)}) collective-permute-start(bf16[128,512]{1,0:T(8,128)(2,1)S(1)} %fusion.23), channel_id=1, source_target_pairs={{0,8},{2,10},{4,12},{6,14},{8,0},{10,2},{12,4},{14,6},{1,9},{3,11}... | collective-permute-start | bytes 393224 | tf_op jit(solution)/shard_map/ppermute | solution.py:25
  28.0 1.6 %collective-permute-done.1 = bf16[128,512]{1,0:T(8,128)(2,1)S(1)} collective-permute-done((bf16[128,512]{1,0:T(8,128)(2,1)S(1)}, bf16[128,512]{1,0:T(8,128)(2,1)S(1)}, u32[]{:S(2)}, u32[]{:S(2)}) %collective-permute-start.1) | collective-permute-done | bytes 131104 | tf_op jit(solution)/shard_map/ppermute | solution.py:25
  29.6 2.5 %collective-permute-start.2 = (bf16[128,512]{1,0:T(8,128)(2,1)S(1)}, bf16[128,512]{1,0:T(8,128)(2,1)S(1)}, u32[]{:S(2)}, u32[]{:S(2)}) collective-permute-start(bf16[128,512]{1,0:T(8,128)(2,1)S(1)} %fusion.22), channel_id=1, source_target_pairs={{0,8},{2,10},{4,12},{6,14},{8,0},{10,2},{12,4},{14,6},{1,9},{3,11}... | collective-permute-start | bytes 393224 | tf_op jit(solution)/shard_map/ppermute | solution.py:25
  32.2 4.6 %collective-permute-done.7 = bf16[128,512]{1,0:T(8,128)(2,1)S(1)} collective-permute-done((bf16[128,512]{1,0:T(8,128)(2,1)S(1)}, bf16[128,512]{1,0:T(8,128)(2,1)S(1)}, u32[]{:S(2)}, u32[]{:S(2)}) %collective-permute-start.7) | collective-permute-done | bytes 131104 | tf_op jit(solution)/shard_map/ppermute | solution.py:25
  36.7 0.1 multiply_convert_fusion
  36.8 1.0 %collective-permute-start.8 = (bf16[128,512]{1,0:T(8,128)(2,1)S(1)}, bf16[128,512]{1,0:T(8,128)(2,1)S(1)}, u32[]{:S(2)}, u32[]{:S(2)}) collective-permute-start(bf16[128,512]{1,0:T(8,128)(2,1)S(1)} %multiply_convert_fusion), channel_id=1, source_target_pairs={{0,4},{2,6},{4,0},{6,2},{8,12},{10,14},{12,8},{14,10},{1,5},{3,7},... | collective-permute-start | bytes 393224 | tf_op jit(solution)/shard_map/ppermute | solution.py:25
  37.8 1.0 %collective-permute-done.2 = bf16[128,512]{1,0:T(8,128)(2,1)S(1)} collective-permute-done((bf16[128,512]{1,0:T(8,128)(2,1)S(1)}, bf16[128,512]{1,0:T(8,128)(2,1)S(1)}, u32[]{:S(2)}, u32[]{:S(2)}) %collective-permute-start.2) | collective-permute-done | bytes 131104 | tf_op jit(solution)/shard_map/ppermute | solution.py:25
  38.8 0.1 multiply_convert_fusion.1
  38.9 0.3 collective-permute-start.3
  39.2 3.4 %collective-permute-done.8 = bf16[128,512]{1,0:T(8,128)(2,1)S(1)} collective-permute-done((bf16[128,512]{1,0:T(8,128)(2,1)S(1)}, bf16[128,512]{1,0:T(8,128)(2,1)S(1)}, u32[]{:S(2)}, u32[]{:S(2)}) %collective-permute-start.8) | collective-permute-done | bytes 131104 | tf_op jit(solution)/shard_map/ppermute | solution.py:25
  42.7 1.5 %collective-permute-start.9 = (bf16[128,1024]{1,0:T(8,128)(2,1)S(1)}, bf16[128,1024]{1,0:T(8,128)(2,1)S(1)}, u32[]{:S(2)}, u32[]{:S(2)}) collective-permute-start(bf16[128,1024]{1,0:T(8,128)(2,1)S(1)} %pad_maximum_fusion.1), channel_id=1, source_target_pairs={{0,2},{2,0},{4,6},{6,4},{8,10},{10,8},{12,14},{14,12},{1,3},{3,1},... | collective-permute-start | bytes 786440 | tf_op jit(solution)/shard_map/ppermute | solution.py:25
  44.2 1.3 %collective-permute-start.4 = (bf16[128,1024]{1,0:T(8,128)(2,1)S(1)}, bf16[128,1024]{1,0:T(8,128)(2,1)S(1)}, u32[]{:S(2)}, u32[]{:S(2)}) collective-permute-start(bf16[128,1024]{1,0:T(8,128)(2,1)S(1)} %pad_maximum_fusion), channel_id=1, source_target_pairs={{0,2},{2,0},{4,6},{6,4},{8,10},{10,8},{12,14},{14,12},{1,3},{3,1},... | collective-permute-start | bytes 786440 | tf_op jit(solution)/shard_map/ppermute | solution.py:25
  45.6 4.9 %collective-permute-done.9 = bf16[128,1024]{1,0:T(8,128)(2,1)S(1)} collective-permute-done((bf16[128,1024]{1,0:T(8,128)(2,1)S(1)}, bf16[128,1024]{1,0:T(8,128)(2,1)S(1)}, u32[]{:S(2)}, u32[]{:S(2)}) %collective-permute-start.9) | collective-permute-done | bytes 262176 | tf_op jit(solution)/shard_map/ppermute | solution.py:25
  50.5 0.1 broadcast_select_fusion.1
  50.6 0.7 fusion
  51.3 2.0 %collective-permute-done.4 = bf16[128,1024]{1,0:T(8,128)(2,1)S(1)} collective-permute-done((bf16[128,1024]{1,0:T(8,128)(2,1)S(1)}, bf16[128,1024]{1,0:T(8,128)(2,1)S(1)}, u32[]{:S(2)}, u32[]{:S(2)}) %collective-permute-start.4) | collective-permute-done | bytes 262176 | tf_op jit(solution)/shard_map/ppermute | solution.py:25
  53.3 0.1 broadcast_select_fusion.3
  53.4 0.7 fusion.7.mine_ref
  54.2 1.5 %collective-permute-done.10.other_ref = f32[512,128]{1,0:T(8,128)S(1)} collective-permute-done((f32[512,128]{1,0:T(8,128)S(1)}, f32[512,128]{1,0:T(8,128)S(1)}, u32[]{:S(2)}, u32[]{:S(2)}) %collective-permute-start.10) | collective-permute-done | bytes 262176 | tf_op jit(solution)/shard_map/ppermute | solution.py:25
  55.7 0.6 fusion.18
  56.4 1.4 %collective-permute-start.11 = (f32[128,128]{1,0:T(8,128)S(1)}, f32[128,128]{1,0:T(8,128)S(1)}, u32[]{:S(2)}, u32[]{:S(2)}) collective-permute-start(f32[128,128]{1,0:T(8,128)S(1)} %fusion.18), channel_id=1, source_target_pairs={{0,2},{2,0},{4,6},{6,4},{8,10},{10,8},{12,14},{14,12},{1,3},{3,1},... | collective-permute-start | bytes 196616 | tf_op jit(solution)/shard_map/ppermute | solution.py:25
  57.7 3.0 %collective-permute-done.11 = f32[128,128]{1,0:T(8,128)S(1)} collective-permute-done((f32[128,128]{1,0:T(8,128)S(1)}, f32[128,128]{1,0:T(8,128)S(1)}, u32[]{:S(2)}, u32[]{:S(2)}) %collective-permute-start.11) | collective-permute-done | bytes 65568 | tf_op jit(solution)/shard_map/ppermute | solution.py:25
  60.7 0.5 collective-permute-start.12
  61.2 3.8 %collective-permute-done.12 = f32[128,128]{1,0:T(8,128)S(1)} collective-permute-done((f32[128,128]{1,0:T(8,128)S(1)}, f32[128,128]{1,0:T(8,128)S(1)}, u32[]{:S(2)}, u32[]{:S(2)}) %collective-permute-start.12) | collective-permute-done | bytes 65568 | tf_op jit(solution)/shard_map/ppermute | solution.py:25
  65.0 2.5 %collective-permute-start.13 = (f32[128,128]{1,0:T(8,128)S(1)}, f32[128,128]{1,0:T(8,128)S(1)}, u32[]{:S(2)}, u32[]{:S(2)}) collective-permute-start(f32[128,128]{1,0:T(8,128)S(1)} %add.95), channel_id=1, source_target_pairs={{0,8},{2,10},{4,12},{6,14},{8,0},{10,2},{12,4},{14,6},{1,9},{3,11}... | collective-permute-start | bytes 196616 | tf_op jit(solution)/shard_map/ppermute | solution.py:25
  67.5 3.5 %collective-permute-done.13 = f32[128,128]{1,0:T(8,128)S(1)} collective-permute-done((f32[128,128]{1,0:T(8,128)S(1)}, f32[128,128]{1,0:T(8,128)S(1)}, u32[]{:S(2)}, u32[]{:S(2)}) %collective-permute-start.13) | collective-permute-done | bytes 65568 | tf_op jit(solution)/shard_map/ppermute | solution.py:25
  71.0 2.2 %copy-done.1 = bf16[512,4096]{1,0:T(8,128)(2,1)S(1)} copy-done((bf16[512,4096]{1,0:T(8,128)(2,1)S(1)}, bf16[512,4096]{1,0:T(8,128)(2,1)}, u32[]{:S(2)}) %copy-start.1) | copy-done | bytes 4194328
  73.2 4.4 %make_basis.1 = (f32[512,128]{1,0:T(8,128)}, f32[128,4096]{1,0:T(8,128)S(1)}) custom-call(f32[128,128]{1,0:T(8,128)S(1)} %add.96.gram_ref, f32[512,128]{1,0:T(8,128)S(1)} %fusion.7.mine_ref, f32[512,128]{1,0:T(8,128)S(1)} %collective-permute-done.10.other_ref, bf16[512,4096]{1,0:T(8,128)(2,1)S(1)} %copy-done.1), custom_call_target="tpu_custom_call" | custom-call | tf_op jit(solution)/shard_map/make_basis/pallas_call | solution.py:233
  77.6 0.1 fusion.27
  77.8 1.4 %collective-permute-start.18 = (bf16[4,16,2048]{2,1,0:T(8,128)(2,1)S(1)}, bf16[4,16,2048]{2,1,0:T(8,128)(2,1)S(1)}, u32[]{:S(2)}, u32[]{:S(2)}) collective-permute-start(bf16[4,16,2048]{2,1,0:T(8,128)(2,1)S(1)} %fusion.17), channel_id=1, source_target_pairs={{0,2},{2,0},{4,6},{6,4},{8,10},{10,8},{12,14},{14,12},{1,3},{3,1},... | collective-permute-start | bytes 786440 | tf_op jit(solution)/shard_map/ppermute | solution.py:25
  79.2 0.8 collective-permute-start.14
  80.0 4.9 %collective-permute-done.18 = bf16[4,16,2048]{2,1,0:T(8,128)(2,1)S(1)} collective-permute-done((bf16[4,16,2048]{2,1,0:T(8,128)(2,1)S(1)}, bf16[4,16,2048]{2,1,0:T(8,128)(2,1)S(1)}, u32[]{:S(2)}, u32[]{:S(2)}) %collective-permute-start.18) | collective-permute-done | bytes 262176 | tf_op jit(solution)/shard_map/ppermute | solution.py:25
  85.0 4.0 %collective-permute-start.21 = (bf16[1,16,2048]{2,1,0:T(8,128)(2,1)S(1)}, bf16[1,16,2048]{2,1,0:T(8,128)(2,1)S(1)}, u32[]{:S(2)}, u32[]{:S(2)}) collective-permute-start(bf16[1,16,2048]{2,1,0:T(8,128)(2,1)S(1)} %get-tuple-element.18), channel_id=1, source_target_pairs={{0,12},{2,14},{4,8},{6,10},{8,4},{10,6},{12,0},{14,2},{1,13},{3,15... | collective-permute-start | bytes 196616 | tf_op jit(solution)/shard_map/ppermute | solution.py:25
  89.0 0.6 collective-permute-start.19
  89.8 3.8 %collective-permute-start.17 = (bf16[1,16,2048]{2,1,0:T(8,128)(2,1)S(1)}, bf16[1,16,2048]{2,1,0:T(8,128)(2,1)S(1)}, u32[]{:S(2)}, u32[]{:S(2)}) collective-permute-start(bf16[1,16,2048]{2,1,0:T(8,128)(2,1)S(1)} %get-tuple-element.15), channel_id=1, source_target_pairs={{0,12},{2,14},{4,8},{6,10},{8,4},{10,6},{12,0},{14,2},{1,13},{3,15... | collective-permute-start | bytes 196616 | tf_op jit(solution)/shard_map/ppermute | solution.py:25
  93.6 0.6 collective-permute-start.15
  94.3 2.1 %collective-permute-done.17 = bf16[1,16,2048]{2,1,0:T(8,128)(2,1)S(1)} collective-permute-done((bf16[1,16,2048]{2,1,0:T(8,128)(2,1)S(1)}, bf16[1,16,2048]{2,1,0:T(8,128)(2,1)S(1)}, u32[]{:S(2)}, u32[]{:S(2)}) %collective-permute-start.17) | collective-permute-done | bytes 65568 | tf_op jit(solution)/shard_map/ppermute | solution.py:25
  96.3 2.4 %collective-permute-done.16 = bf16[1,16,2048]{2,1,0:T(8,128)(2,1)S(1)} collective-permute-done((bf16[1,16,2048]{2,1,0:T(8,128)(2,1)S(1)}, bf16[1,16,2048]{2,1,0:T(8,128)(2,1)S(1)}, u32[]{:S(2)}, u32[]{:S(2)}) %collective-permute-start.16) | collective-permute-done | bytes 65568 | tf_op jit(solution)/shard_map/ppermute | solution.py:25
  98.8 0.7 pad_maximum_fusion.2
  (37 shorter events, 0.8 us)
Async XLA Ops:
  3.8 7.3 %copy-start.2 = (bf16[128,1024]{1,0:T(8,128)(2,1)S(1)}, bf16[128,1024]{1,0:T(8,128)(2,1)}, u32[]{:S(2)}) copy-start(bf16[128,1024]{1,0:T(8,128)(2,1)} %sketch_halves.2.refs_0_) | copy-start | bytes 786436
  8.1 15.2 %copy-start.3 = (f32[128,1024]{1,0:T(8,128)S(1)}, f32[128,1024]{1,0:T(8,128)}, u32[]{:S(2)}) copy-start(f32[128,1024]{1,0:T(8,128)} %get-tuple-element.7) | copy-start | bytes 1572868
  8.1 10.3 %collective-permute-start.5 = (bf16[128,1024]{1,0:T(8,128)(2,1)}, bf16[128,1024]{1,0:T(8,128)(2,1)S(1)}, u32[]{:S(2)}, u32[]{:S(2)}) collective-permute-start(bf16[128,1024]{1,0:T(8,128)(2,1)} %get-tuple-element.9), channel_id=1, source_target_pairs={{0,2},{2,0},{4,6},{6,4},{8,10},{10,8},{12,14},{14,12},{1,3},{3,1},... | collective-permute-start | bytes 786440 | tf_op jit(solution)/shard_map/ppermute | solution.py:25
  11.1 12.1 %collective-permute-start = (bf16[128,1024]{1,0:T(8,128)(2,1)S(1)}, bf16[128,1024]{1,0:T(8,128)(2,1)S(1)}, u32[]{:S(2)}, u32[]{:S(2)}) collective-permute-start(bf16[128,1024]{1,0:T(8,128)(2,1)S(1)} %copy-done.2), channel_id=1, source_target_pairs={{0,2},{2,0},{4,6},{6,4},{8,10},{10,8},{12,14},{14,12},{1,3},{3,1},... | collective-permute-start | bytes 786440 | tf_op jit(solution)/shard_map/ppermute | solution.py:25
  19.6 5.7 %collective-permute-start.6 = (bf16[128,512]{1,0:T(8,128)(2,1)S(1)}, bf16[128,512]{1,0:T(8,128)(2,1)S(1)}, u32[]{:S(2)}, u32[]{:S(2)}) collective-permute-start(bf16[128,512]{1,0:T(8,128)(2,1)S(1)} %select_convert_fusion), channel_id=1, source_target_pairs={{0,4},{2,6},{4,0},{6,2},{8,12},{10,14},{12,8},{14,10},{1,5},{3,7},... | collective-permute-start | bytes 393224 | tf_op jit(solution)/shard_map/ppermute | solution.py:25
  23.4 6.2 %collective-permute-start.1 = (bf16[128,512]{1,0:T(8,128)(2,1)S(1)}, bf16[128,512]{1,0:T(8,128)(2,1)S(1)}, u32[]{:S(2)}, u32[]{:S(2)}) collective-permute-start(bf16[128,512]{1,0:T(8,128)(2,1)S(1)} %select_convert_fusion.1), channel_id=1, source_target_pairs={{0,4},{2,6},{4,0},{6,2},{8,12},{10,14},{12,8},{14,10},{1,5},{3,7},... | collective-permute-start | bytes 393224 | tf_op jit(solution)/shard_map/ppermute | solution.py:25
  25.3 11.4 %collective-permute-start.7 = (bf16[128,512]{1,0:T(8,128)(2,1)S(1)}, bf16[128,512]{1,0:T(8,128)(2,1)S(1)}, u32[]{:S(2)}, u32[]{:S(2)}) collective-permute-start(bf16[128,512]{1,0:T(8,128)(2,1)S(1)} %fusion.23), channel_id=1, source_target_pairs={{0,8},{2,10},{4,12},{6,14},{8,0},{10,2},{12,4},{14,6},{1,9},{3,11}... | collective-permute-start | bytes 393224 | tf_op jit(solution)/shard_map/ppermute | solution.py:25
  29.6 9.2 %collective-permute-start.2 = (bf16[128,512]{1,0:T(8,128)(2,1)S(1)}, bf16[128,512]{1,0:T(8,128)(2,1)S(1)}, u32[]{:S(2)}, u32[]{:S(2)}) collective-permute-start(bf16[128,512]{1,0:T(8,128)(2,1)S(1)} %fusion.22), channel_id=1, source_target_pairs={{0,8},{2,10},{4,12},{6,14},{8,0},{10,2},{12,4},{14,6},{1,9},{3,11}... | collective-permute-start | bytes 393224 | tf_op jit(solution)/shard_map/ppermute | solution.py:25
  36.7 13.9 %copy-start = (bf16[512,4096]{1,0:T(8,128)(2,1)S(1)}, bf16[512,4096]{1,0:T(8,128)(2,1)}, u32[]{:S(2)}) copy-start(bf16[512,4096]{1,0:T(8,128)(2,1)} %slab_ref.5) | copy-start | bytes 12582916
  36.8 5.8 %collective-permute-start.8 = (bf16[128,512]{1,0:T(8,128)(2,1)S(1)}, bf16[128,512]{1,0:T(8,128)(2,1)S(1)}, u32[]{:S(2)}, u32[]{:S(2)}) collective-permute-start(bf16[128,512]{1,0:T(8,128)(2,1)S(1)} %multiply_convert_fusion), channel_id=1, source_target_pairs={{0,4},{2,6},{4,0},{6,2},{8,12},{10,14},{12,8},{14,10},{1,5},{3,7},... | collective-permute-start | bytes 393224 | tf_op jit(solution)/shard_map/ppermute | solution.py:25
  38.9 5.2 %collective-permute-start.3 = (bf16[128,512]{1,0:T(8,128)(2,1)S(1)}, bf16[128,512]{1,0:T(8,128)(2,1)S(1)}, u32[]{:S(2)}, u32[]{:S(2)}) collective-permute-start(bf16[128,512]{1,0:T(8,128)(2,1)S(1)} %multiply_convert_fusion.1), channel_id=1, source_target_pairs={{0,4},{2,6},{4,0},{6,2},{8,12},{10,14},{12,8},{14,10},{1,5},{3,7},... | collective-permute-start | bytes 393224 | tf_op jit(solution)/shard_map/ppermute | solution.py:25
  42.7 7.8 %collective-permute-start.9 = (bf16[128,1024]{1,0:T(8,128)(2,1)S(1)}, bf16[128,1024]{1,0:T(8,128)(2,1)S(1)}, u32[]{:S(2)}, u32[]{:S(2)}) collective-permute-start(bf16[128,1024]{1,0:T(8,128)(2,1)S(1)} %pad_maximum_fusion.1), channel_id=1, source_target_pairs={{0,2},{2,0},{4,6},{6,4},{8,10},{10,8},{12,14},{14,12},{1,3},{3,1},... | collective-permute-start | bytes 786440 | tf_op jit(solution)/shard_map/ppermute | solution.py:25
  44.2 9.1 %collective-permute-start.4 = (bf16[128,1024]{1,0:T(8,128)(2,1)S(1)}, bf16[128,1024]{1,0:T(8,128)(2,1)S(1)}, u32[]{:S(2)}, u32[]{:S(2)}) collective-permute-start(bf16[128,1024]{1,0:T(8,128)(2,1)S(1)} %pad_maximum_fusion), channel_id=1, source_target_pairs={{0,2},{2,0},{4,6},{6,4},{8,10},{10,8},{12,14},{14,12},{1,3},{3,1},... | collective-permute-start | bytes 786440 | tf_op jit(solution)/shard_map/ppermute | solution.py:25
  54.1 1.6 %collective-permute-start.10 = (f32[512,128]{1,0:T(8,128)S(1)}, f32[512,128]{1,0:T(8,128)S(1)}, u32[]{:S(2)}, u32[]{:S(2)}) collective-permute-start(f32[512,128]{1,0:T(8,128)S(1)} %fusion.7.mine_ref), channel_id=1, source_target_pairs={{0,1},{1,0},{2,3},{3,2},{4,5},{5,4},{6,7},{7,6},{8,9},{9,8},{10,11... | collective-permute-start | bytes 786440 | tf_op jit(solution)/shard_map/ppermute | solution.py:25
  56.4 4.3 %collective-permute-start.11 = (f32[128,128]{1,0:T(8,128)S(1)}, f32[128,128]{1,0:T(8,128)S(1)}, u32[]{:S(2)}, u32[]{:S(2)}) collective-permute-start(f32[128,128]{1,0:T(8,128)S(1)} %fusion.18), channel_id=1, source_target_pairs={{0,2},{2,0},{4,6},{6,4},{8,10},{10,8},{12,14},{14,12},{1,3},{3,1},... | collective-permute-start | bytes 196616 | tf_op jit(solution)/shard_map/ppermute | solution.py:25
  60.7 4.3 %collective-permute-start.12 = (f32[128,128]{1,0:T(8,128)S(1)}, f32[128,128]{1,0:T(8,128)S(1)}, u32[]{:S(2)}, u32[]{:S(2)}) collective-permute-start(f32[128,128]{1,0:T(8,128)S(1)} %add.94), channel_id=1, source_target_pairs={{0,4},{2,6},{4,0},{6,2},{8,12},{10,14},{12,8},{14,10},{1,5},{3,7},... | collective-permute-start | bytes 196616 | tf_op jit(solution)/shard_map/ppermute | solution.py:25
  65.0 5.9 %collective-permute-start.13 = (f32[128,128]{1,0:T(8,128)S(1)}, f32[128,128]{1,0:T(8,128)S(1)}, u32[]{:S(2)}, u32[]{:S(2)}) collective-permute-start(f32[128,128]{1,0:T(8,128)S(1)} %add.95), channel_id=1, source_target_pairs={{0,8},{2,10},{4,12},{6,14},{8,0},{10,2},{12,4},{14,6},{1,9},{3,11}... | collective-permute-start | bytes 196616 | tf_op jit(solution)/shard_map/ppermute | solution.py:25
  71.0 2.2 %copy-start.1 = (bf16[512,4096]{1,0:T(8,128)(2,1)S(1)}, bf16[512,4096]{1,0:T(8,128)(2,1)}, u32[]{:S(2)}) copy-start(bf16[512,4096]{1,0:T(8,128)(2,1)} %slab_ref.5) | copy-start | bytes 12582916
  77.8 7.1 %collective-permute-start.18 = (bf16[4,16,2048]{2,1,0:T(8,128)(2,1)S(1)}, bf16[4,16,2048]{2,1,0:T(8,128)(2,1)S(1)}, u32[]{:S(2)}, u32[]{:S(2)}) collective-permute-start(bf16[4,16,2048]{2,1,0:T(8,128)(2,1)S(1)} %fusion.17), channel_id=1, source_target_pairs={{0,2},{2,0},{4,6},{6,4},{8,10},{10,8},{12,14},{14,12},{1,3},{3,1},... | collective-permute-start | bytes 786440 | tf_op jit(solution)/shard_map/ppermute | solution.py:25
  79.2 10.5 %collective-permute-start.14 = (bf16[4,16,2048]{2,1,0:T(8,128)(2,1)S(1)}, bf16[4,16,2048]{2,1,0:T(8,128)(2,1)S(1)}, u32[]{:S(2)}, u32[]{:S(2)}) collective-permute-start(bf16[4,16,2048]{2,1,0:T(8,128)(2,1)S(1)} %fusion.16), channel_id=1, source_target_pairs={{0,2},{2,0},{4,6},{6,4},{8,10},{10,8},{12,14},{14,12},{1,3},{3,1},... | collective-permute-start | bytes 786440 | tf_op jit(solution)/shard_map/ppermute | solution.py:25
  85.0 8.6 %collective-permute-start.21 = (bf16[1,16,2048]{2,1,0:T(8,128)(2,1)S(1)}, bf16[1,16,2048]{2,1,0:T(8,128)(2,1)S(1)}, u32[]{:S(2)}, u32[]{:S(2)}) collective-permute-start(bf16[1,16,2048]{2,1,0:T(8,128)(2,1)S(1)} %get-tuple-element.18), channel_id=1, source_target_pairs={{0,12},{2,14},{4,8},{6,10},{8,4},{10,6},{12,0},{14,2},{1,13},{3,15... | collective-permute-start | bytes 196616 | tf_op jit(solution)/shard_map/ppermute | solution.py:25
  89.0 5.2 %collective-permute-start.20 = (bf16[1,16,2048]{2,1,0:T(8,128)(2,1)S(1)}, bf16[1,16,2048]{2,1,0:T(8,128)(2,1)S(1)}, u32[]{:S(2)}, u32[]{:S(2)}) collective-permute-start(bf16[1,16,2048]{2,1,0:T(8,128)(2,1)S(1)} %get-tuple-element.19), channel_id=1, source_target_pairs={{0,8},{2,10},{4,12},{6,14},{8,0},{10,2},{12,4},{14,6},{1,9},{3,11}... | collective-permute-start | bytes 196616 | tf_op jit(solution)/shard_map/ppermute | solution.py:25
  89.0 5.2 %collective-permute-start.19 = (bf16[1,16,2048]{2,1,0:T(8,128)(2,1)S(1)}, bf16[1,16,2048]{2,1,0:T(8,128)(2,1)S(1)}, u32[]{:S(2)}, u32[]{:S(2)}) collective-permute-start(bf16[1,16,2048]{2,1,0:T(8,128)(2,1)S(1)} %get-tuple-element.17), channel_id=1, source_target_pairs={{0,4},{2,6},{4,0},{6,2},{8,12},{10,14},{12,8},{14,10},{1,5},{3,7},... | collective-permute-start | bytes 196616 | tf_op jit(solution)/shard_map/ppermute | solution.py:25
  89.8 6.6 %collective-permute-start.17 = (bf16[1,16,2048]{2,1,0:T(8,128)(2,1)S(1)}, bf16[1,16,2048]{2,1,0:T(8,128)(2,1)S(1)}, u32[]{:S(2)}, u32[]{:S(2)}) collective-permute-start(bf16[1,16,2048]{2,1,0:T(8,128)(2,1)S(1)} %get-tuple-element.15), channel_id=1, source_target_pairs={{0,12},{2,14},{4,8},{6,10},{8,4},{10,6},{12,0},{14,2},{1,13},{3,15... | collective-permute-start | bytes 196616 | tf_op jit(solution)/shard_map/ppermute | solution.py:25
  93.6 5.2 %collective-permute-start.16 = (bf16[1,16,2048]{2,1,0:T(8,128)(2,1)S(1)}, bf16[1,16,2048]{2,1,0:T(8,128)(2,1)S(1)}, u32[]{:S(2)}, u32[]{:S(2)}) collective-permute-start(bf16[1,16,2048]{2,1,0:T(8,128)(2,1)S(1)} %get-tuple-element.16), channel_id=1, source_target_pairs={{0,8},{2,10},{4,12},{6,14},{8,0},{10,2},{12,4},{14,6},{1,9},{3,11}... | collective-permute-start | bytes 196616 | tf_op jit(solution)/shard_map/ppermute | solution.py:25
  93.6 5.2 %collective-permute-start.15 = (bf16[1,16,2048]{2,1,0:T(8,128)(2,1)S(1)}, bf16[1,16,2048]{2,1,0:T(8,128)(2,1)S(1)}, u32[]{:S(2)}, u32[]{:S(2)}) collective-permute-start(bf16[1,16,2048]{2,1,0:T(8,128)(2,1)S(1)} %get-tuple-element.14), channel_id=1, source_target_pairs={{0,4},{2,6},{4,0},{6,2},{8,12},{10,14},{12,8},{14,10},{1,5},{3,7},... | collective-permute-start | bytes 196616 | tf_op jit(solution)/shard_map/ppermute | solution.py:25

commit v7 on v4

--- a/solution.py
+++ b/solution.py
@@ -54,23 +54,34 @@
     return blocks[0]
 
 
-def gather_level(blocks, axis, stride, radix):
-    digit = digit_of(axis, stride, radix)
-    held = [blocks] + [swap(blocks, axis, t * stride) for t in range(1, radix)]
-    bit = 1
-    while bit < radix:
-        flip = jnp.bitwise_and(digit, bit) != 0
-        held = [jnp.where(flip, held[j ^ bit], held[j]) for j in range(radix)]
-        bit *= 2
-    whole = jnp.stack(held, axis=1)
-    return whole.reshape((blocks.shape[0] * radix,) + blocks.shape[1:])
-
-
-def gather(block, axis):
-    blocks = block[None]
-    for stride, radix in reversed(levels_of(lax.axis_size(axis))):
-        blocks = gather_level(blocks, axis, stride, radix)
-    return blocks
+def bit_of(axis, bit):
+    return lax.rem(lax.div(lax.axis_index(axis), 1 << bit), 2)
+
+
+def sum_and_share(value, axis, order, scale):
+    for bit in order[:-1]:
+        upper = bit_of(axis, bit) == 1
+        half = value.shape[0] // 2
+        low, high = value[:half], value[half:]
+        send = jnp.where(upper, low, high).astype(jnp.bfloat16)
+        landed = swap(send, axis, 1 << bit)
+        value = jnp.where(upper, high, low) + landed.astype(jnp.float32)
+    landed = swap(value.astype(jnp.bfloat16), axis, 1 << order[-1])
+    block = ((value + landed.astype(jnp.float32)) * scale).astype(jnp.bfloat16)
+    for bit in reversed(order[:-1]):
+        upper = bit_of(axis, bit) == 1
+        other = swap(block, axis, 1 << bit)
+        block = jnp.concatenate(
+            [jnp.where(upper, other, block), jnp.where(upper, block, other)], axis=0
+        )
+    return block
+
+
+def orders_of(axis):
+    bits = list(range((lax.axis_size(axis) - 1).bit_length()))
+    if len(bits) < 3:
+        return [bits, bits]
+    return [bits, [bits[1], bits[0]] + bits[2:]]
 
 
 def matmul(left, right, exact=True):
@@ -197,18 +208,16 @@
     spans = [slice(c * cols_chunk, (c + 1) * cols_chunk) for c in range(CHUNKS)]
 
     partial_sketch = 0.0
-    for span in spans:
+    for span, order in zip(spans, orders_of("row")):
         local_cols = lax.dot_general(
             activations[:, span],
             start_sketch,
             (((0,), (0,)), ((), ())),
             preferred_element_type=jnp.float32,
         )
-        share = scatter_sum(local_cols.reshape(parts, cols_chunk // parts, width), "row")
-        chunk = gather((share / root_rows).astype(jnp.bfloat16), "row")
         partial_sketch = partial_sketch + jnp.dot(
             activations[:, span],
-            chunk.reshape(cols_chunk, width),
+            sum_and_share(local_cols, "row", order, 1.0 / root_rows),
             preferred_element_type=jnp.float32,
         )
     other_sketch = swap(partial_sketch, "col", 1)

time: 92.3 us -> 92.2 us (level)
  starting transfers between devices: 36.7 us -> 30 us
  waiting for transfers between devices: 40.5 us -> 44.9 us
  local copies, waits for them, and re-layouts: 1.37 us -> 3.34 us
    ppermute x28 -> x22, starting transfers between devices: 36.7 us -> 30 us  [swap(): return lax.ppermute(value, axis, [(i, i ^ distance) for i in range(size)])]
    ppermute x28 -> x22, waiting for transfers between devices: 40.5 us -> 44.9 us  [swap(): return lax.ppermute(value, axis, [(i, i ^ distance) for i in range(size)])]
    unnamed x4 -> x6, local copies, waits for them, and re-layouts: 0.9 us -> 3.07 us
  transfers between devices with their start and end apart: 28 -> 22, of which waited for: 16 -> 17; matrix products, arithmetic and copies ran while one was open for 4% -> 4% of each run, Pallas kernels for 0% -> 0%
where the time goes in v7:
time: 92.2 us; the launch traced here: 92 us
  waiting for transfers between devices  44.9 us (49%)
  starting transfers between devices  30 us (33%)
  matrix products  6.68 us (7%)
  Pallas kernels  4.43 us (5%)
  local copies, waits for them, and re-layouts  3.34 us (4%)
  other arithmetic  1.72 us (2%)
    ppermute x22, waiting for transfers between devices, swap(): return lax.ppermute(value, axis, [(i, i ^ distance) for i in range(size)])  44.9 us
    ppermute x22, starting transfers between devices, swap(): return lax.ppermute(value, axis, [(i, i ^ distance) for i in range(size)])  30 us
    dot_general x2, matrix products, per_device(): lax.dot_general(activations[:, span], start_sketch, (((0,), (0,)), ((), (...  4.65 us
    pallas_call x1, Pallas kernels, make_basis(): pl.pallas_call(functools.partial(basis_kernel, total_cols, root_rows), ou...  4.43 us
    unnamed x6, local copies, waits for them, and re-layouts  3.07 us
  transfers between devices with their start and end apart: 22, of which 17 were waited for; matrix products, arithmetic and copies ran while one was open for 4% of the time, Pallas kernels for 0%

profile of v7, /device:TPU:0, one launch (start us, length us, event | category | flops | bytes accessed | tf_op | source)
XLA Modules:
  0.0 92.0 jit_solution(8875343589118122882)
XLA Ops:
  0.7 0.9 copy-done
  1.5 2.3 %fusion.2 = f32[2048,128]{1,0:T(8,128)S(1)} fusion(bf16[512,128]{1,0:T(8,128)(2,1)S(1)} %copy-done, bf16[512,4096]{1,0:T(8,128)(2,1)} %slab_ref.1), kind=kOutput, calls=%fused_computation.2 | convolution fusion | flops 268435456 | bytes 3276800 | tf_op jit(solution)/shard_map/dot_general | solution.py:212
  3.9 3.1 %collective-permute-start.5 = (bf16[1024,128]{1,0:T(8,128)(2,1)S(1)}, bf16[1024,128]{1,0:T(8,128)(2,1)S(1)}, u32[]{:S(2)}, u32[]{:S(2)}) collective-permute-start(bf16[1024,128]{1,0:T(8,128)(2,1)S(1)} %select_convert_fusion), channel_id=1, source_target_pairs={{0,4},{2,6},{4,0},{6,2},{8,12},{10,14},{12,8},{14,10},{1,5},{3,7},... | collective-permute-start | bytes 786440 | tf_op jit(solution)/shard_map/ppermute | solution.py:25
  7.0 2.3 %fusion.6 = f32[2048,128]{1,0:T(8,128)S(1)} fusion(bf16[512,128]{1,0:T(8,128)(2,1)S(1)} %copy-done, bf16[512,4096]{1,0:T(8,128)(2,1)} %slab_ref.1), kind=kOutput, calls=%fused_computation.6 | convolution fusion | flops 268435456 | bytes 3276800 | tf_op jit(solution)/shard_map/dot_general | solution.py:212
  9.4 1.6 %collective-permute-start = (bf16[1024,128]{1,0:T(8,128)(2,1)S(1)}, bf16[1024,128]{1,0:T(8,128)(2,1)S(1)}, u32[]{:S(2)}, u32[]{:S(2)}) collective-permute-start(bf16[1024,128]{1,0:T(8,128)(2,1)S(1)} %select_convert_fusion.1), channel_id=1, source_target_pairs={{0,2},{2,0},{4,6},{6,4},{8,10},{10,8},{12,14},{14,12},{1,3},{3,1},... | collective-permute-start | bytes 786440 | tf_op jit(solution)/shard_map/ppermute | solution.py:25
  11.0 2.4 %collective-permute-done.5 = bf16[1024,128]{1,0:T(8,128)(2,1)S(1)} collective-permute-done((bf16[1024,128]{1,0:T(8,128)(2,1)S(1)}, bf16[1024,128]{1,0:T(8,128)(2,1)S(1)}, u32[]{:S(2)}, u32[]{:S(2)}) %collective-permute-start.5) | collective-permute-done | bytes 262176 | tf_op jit(solution)/shard_map/ppermute | solution.py:25
  13.4 1.7 %collective-permute-start.6 = (bf16[512,128]{1,0:T(8,128)(2,1)S(1)}, bf16[512,128]{1,0:T(8,128)(2,1)S(1)}, u32[]{:S(2)}, u32[]{:S(2)}) collective-permute-start(bf16[512,128]{1,0:T(8,128)(2,1)S(1)} %select_convert_fusion.2), channel_id=1, source_target_pairs={{0,2},{2,0},{4,6},{6,4},{8,10},{10,8},{12,14},{14,12},{1,3},{3,1},... | collective-permute-start | bytes 393224 | tf_op jit(solution)/shard_map/ppermute | solution.py:25
  15.1 3.5 %collective-permute-done = bf16[1024,128]{1,0:T(8,128)(2,1)S(1)} collective-permute-done((bf16[1024,128]{1,0:T(8,128)(2,1)S(1)}, bf16[1024,128]{1,0:T(8,128)(2,1)S(1)}, u32[]{:S(2)}, u32[]{:S(2)}) %collective-permute-start) | collective-permute-done | bytes 262176 | tf_op jit(solution)/shard_map/ppermute | solution.py:25
  18.8 0.1 collective-permute-start.1
  18.8 1.2 %collective-permute-done.6 = bf16[512,128]{1,0:T(8,128)(2,1)S(1)} collective-permute-done((bf16[512,128]{1,0:T(8,128)(2,1)S(1)}, bf16[512,128]{1,0:T(8,128)(2,1)S(1)}, u32[]{:S(2)}, u32[]{:S(2)}) %collective-permute-start.6) | collective-permute-done | bytes 131104 | tf_op jit(solution)/shard_map/ppermute | solution.py:25
  20.1 2.7 %collective-permute-start.7 = (bf16[512,128]{1,0:T(8,128)(2,1)S(1)}, bf16[512,128]{1,0:T(8,128)(2,1)S(1)}, u32[]{:S(2)}, u32[]{:S(2)}) collective-permute-start(bf16[512,128]{1,0:T(8,128)(2,1)S(1)} %fusion.27), channel_id=1, source_target_pairs={{0,8},{2,10},{4,12},{6,14},{8,0},{10,2},{12,4},{14,6},{1,9},{3,11}... | collective-permute-start | bytes 393224 | tf_op jit(solution)/shard_map/ppermute | solution.py:25
  22.7 1.2 %collective-permute-done.1 = bf16[512,128]{1,0:T(8,128)(2,1)S(1)} collective-permute-done((bf16[512,128]{1,0:T(8,128)(2,1)S(1)}, bf16[512,128]{1,0:T(8,128)(2,1)S(1)}, u32[]{:S(2)}, u32[]{:S(2)}) %collective-permute-start.1) | collective-permute-done | bytes 131104 | tf_op jit(solution)/shard_map/ppermute | solution.py:25
  24.0 3.5 %collective-permute-start.2 = (bf16[512,128]{1,0:T(8,128)(2,1)S(1)}, bf16[512,128]{1,0:T(8,128)(2,1)S(1)}, u32[]{:S(2)}, u32[]{:S(2)}) collective-permute-start(bf16[512,128]{1,0:T(8,128)(2,1)S(1)} %fusion.26), channel_id=1, source_target_pairs={{0,8},{2,10},{4,12},{6,14},{8,0},{10,2},{12,4},{14,6},{1,9},{3,11}... | collective-permute-start | bytes 393224 | tf_op jit(solution)/shard_map/ppermute | solution.py:25
  27.5 4.2 %collective-permute-done.7 = bf16[512,128]{1,0:T(8,128)(2,1)S(1)} collective-permute-done((bf16[512,128]{1,0:T(8,128)(2,1)S(1)}, bf16[512,128]{1,0:T(8,128)(2,1)S(1)}, u32[]{:S(2)}, u32[]{:S(2)}) %collective-permute-start.7) | collective-permute-done | bytes 131104 | tf_op jit(solution)/shard_map/ppermute | solution.py:25
  31.7 0.1 multiply_convert_fusion
  31.8 1.6 %collective-permute-start.8 = (bf16[512,128]{1,0:T(8,128)(2,1)S(1)}, bf16[512,128]{1,0:T(8,128)(2,1)S(1)}, u32[]{:S(2)}, u32[]{:S(2)}) collective-permute-start(bf16[512,128]{1,0:T(8,128)(2,1)S(1)} %multiply_convert_fusion), channel_id=1, source_target_pairs={{0,2},{2,0},{4,6},{6,4},{8,10},{10,8},{12,14},{14,12},{1,3},{3,1},... | collective-permute-start | bytes 393224 | tf_op jit(solution)/shard_map/ppermute | solution.py:25
  33.3 0.2 collective-permute-done.2
  33.6 0.1 collective-permute-start.3
  33.7 3.1 %collective-permute-done.8 = bf16[512,128]{1,0:T(8,128)(2,1)S(1)} collective-permute-done((bf16[512,128]{1,0:T(8,128)(2,1)S(1)}, bf16[512,128]{1,0:T(8,128)(2,1)S(1)}, u32[]{:S(2)}, u32[]{:S(2)}) %collective-permute-start.8) | collective-permute-done | bytes 131104 | tf_op jit(solution)/shard_map/ppermute | solution.py:25
  36.9 0.1 collective-permute-start.9
  36.9 3.1 %collective-permute-done.3 = bf16[512,128]{1,0:T(8,128)(2,1)S(1)} collective-permute-done((bf16[512,128]{1,0:T(8,128)(2,1)S(1)}, bf16[512,128]{1,0:T(8,128)(2,1)S(1)}, u32[]{:S(2)}, u32[]{:S(2)}) %collective-permute-start.3) | collective-permute-done | bytes 131104 | tf_op jit(solution)/shard_map/ppermute | solution.py:25
  40.2 1.6 %collective-permute-start.4 = (bf16[1024,128]{1,0:T(8,128)(2,1)S(1)}, bf16[1024,128]{1,0:T(8,128)(2,1)S(1)}, u32[]{:S(2)}, u32[]{:S(2)}) collective-permute-start(bf16[1024,128]{1,0:T(8,128)(2,1)S(1)} %pad_maximum_fusion), channel_id=1, source_target_pairs={{0,2},{2,0},{4,6},{6,4},{8,10},{10,8},{12,14},{14,12},{1,3},{3,1},... | collective-permute-start | bytes 786440 | tf_op jit(solution)/shard_map/ppermute | solution.py:25
  41.7 2.1 %collective-permute-done.9 = bf16[1024,128]{1,0:T(8,128)(2,1)S(1)} collective-permute-done((bf16[1024,128]{1,0:T(8,128)(2,1)S(1)}, bf16[1024,128]{1,0:T(8,128)(2,1)S(1)}, u32[]{:S(2)}, u32[]{:S(2)}) %collective-permute-start.9) | collective-permute-done | bytes 262176 | tf_op jit(solution)/shard_map/ppermute | solution.py:25
  43.8 0.1 broadcast_select_fusion.1
  43.9 0.7 fusion
  44.6 1.9 %collective-permute-done.4 = bf16[1024,128]{1,0:T(8,128)(2,1)S(1)} collective-permute-done((bf16[1024,128]{1,0:T(8,128)(2,1)S(1)}, bf16[1024,128]{1,0:T(8,128)(2,1)S(1)}, u32[]{:S(2)}, u32[]{:S(2)}) %collective-permute-start.4) | collective-permute-done | bytes 262176 | tf_op jit(solution)/shard_map/ppermute | solution.py:25
  46.6 0.1 broadcast_select_fusion.3
  46.7 0.7 fusion.11.mine_ref
  47.5 1.5 %collective-permute-done.10.other_ref = f32[512,128]{1,0:T(8,128)S(1)} collective-permute-done((f32[512,128]{1,0:T(8,128)S(1)}, f32[512,128]{1,0:T(8,128)S(1)}, u32[]{:S(2)}, u32[]{:S(2)}) %collective-permute-start.10) | collective-permute-done | bytes 262176 | tf_op jit(solution)/shard_map/ppermute | solution.py:25
  49.0 0.6 fusion.22
  49.6 1.6 %collective-permute-start.11 = (f32[128,128]{1,0:T(8,128)S(1)}, f32[128,128]{1,0:T(8,128)S(1)}, u32[]{:S(2)}, u32[]{:S(2)}) collective-permute-start(f32[128,128]{1,0:T(8,128)S(1)} %fusion.22), channel_id=1, source_target_pairs={{0,2},{2,0},{4,6},{6,4},{8,10},{10,8},{12,14},{14,12},{1,3},{3,1},... | collective-permute-start | bytes 196616 | tf_op jit(solution)/shard_map/ppermute | solution.py:25
  51.2 2.8 %collective-permute-done.11 = f32[128,128]{1,0:T(8,128)S(1)} collective-permute-done((f32[128,128]{1,0:T(8,128)S(1)}, f32[128,128]{1,0:T(8,128)S(1)}, u32[]{:S(2)}, u32[]{:S(2)}) %collective-permute-start.11) | collective-permute-done | bytes 65568 | tf_op jit(solution)/shard_map/ppermute | solution.py:25
  54.1 4.3 %collective-permute-done.12 = f32[128,128]{1,0:T(8,128)S(1)} collective-permute-done((f32[128,128]{1,0:T(8,128)S(1)}, f32[128,128]{1,0:T(8,128)S(1)}, u32[]{:S(2)}, u32[]{:S(2)}) %collective-permute-start.12) | collective-permute-done | bytes 65568 | tf_op jit(solution)/shard_map/ppermute | solution.py:25
  58.3 1.4 %collective-permute-start.13 = (f32[128,128]{1,0:T(8,128)S(1)}, f32[128,128]{1,0:T(8,128)S(1)}, u32[]{:S(2)}, u32[]{:S(2)}) collective-permute-start(f32[128,128]{1,0:T(8,128)S(1)} %add.95), channel_id=1, source_target_pairs={{0,8},{2,10},{4,12},{6,14},{8,0},{10,2},{12,4},{14,6},{1,9},{3,11}... | collective-permute-start | bytes 196616 | tf_op jit(solution)/shard_map/ppermute | solution.py:25
  59.7 4.4 %collective-permute-done.13 = f32[128,128]{1,0:T(8,128)S(1)} collective-permute-done((f32[128,128]{1,0:T(8,128)S(1)}, f32[128,128]{1,0:T(8,128)S(1)}, u32[]{:S(2)}, u32[]{:S(2)}) %collective-permute-start.13) | collective-permute-done | bytes 65568 | tf_op jit(solution)/shard_map/ppermute | solution.py:25
  64.1 2.2 %copy-done.2 = bf16[512,4096]{1,0:T(8,128)(2,1)S(1)} copy-done((bf16[512,4096]{1,0:T(8,128)(2,1)S(1)}, bf16[512,4096]{1,0:T(8,128)(2,1)}, u32[]{:S(2)}) %copy-start.2) | copy-done | bytes 4194328
  66.3 4.4 %make_basis.1 = (f32[512,128]{1,0:T(8,128)}, f32[128,4096]{1,0:T(8,128)S(1)}) custom-call(f32[128,128]{1,0:T(8,128)S(1)} %add.96.gram_ref, f32[512,128]{1,0:T(8,128)S(1)} %fusion.11.mine_ref, f32[512,128]{1,0:T(8,128)S(1)} %collective-permute-done.10.other_ref, bf16[512,4096]{1,0:T(8,128)(2,1)S(1)} %copy-done.2), custom_call_target="tpu_custom_call" | custom-call | tf_op jit(solution)/shard_map/make_basis/pallas_call | solution.py:182
  70.7 0.1 fusion.31
  70.9 1.6 %collective-permute-start.18 = (bf16[4,16,2048]{2,1,0:T(8,128)(2,1)S(1)}, bf16[4,16,2048]{2,1,0:T(8,128)(2,1)S(1)}, u32[]{:S(2)}, u32[]{:S(2)}) collective-permute-start(bf16[4,16,2048]{2,1,0:T(8,128)(2,1)S(1)} %fusion.21), channel_id=1, source_target_pairs={{0,2},{2,0},{4,6},{6,4},{8,10},{10,8},{12,14},{14,12},{1,3},{3,1},... | collective-permute-start | bytes 786440 | tf_op jit(solution)/shard_map/ppermute | solution.py:25
  72.5 0.6 collective-permute-start.14
  73.1 5.7 %collective-permute-done.18 = bf16[4,16,2048]{2,1,0:T(8,128)(2,1)S(1)} collective-permute-done((bf16[4,16,2048]{2,1,0:T(8,128)(2,1)S(1)}, bf16[4,16,2048]{2,1,0:T(8,128)(2,1)S(1)}, u32[]{:S(2)}, u32[]{:S(2)}) %collective-permute-start.18) | collective-permute-done | bytes 262176 | tf_op jit(solution)/shard_map/ppermute | solution.py:25
  79.0 2.5 %collective-permute-start.21 = (bf16[1,16,2048]{2,1,0:T(8,128)(2,1)S(1)}, bf16[1,16,2048]{2,1,0:T(8,128)(2,1)S(1)}, u32[]{:S(2)}, u32[]{:S(2)}) collective-permute-start(bf16[1,16,2048]{2,1,0:T(8,128)(2,1)S(1)} %get-tuple-element.12), channel_id=1, source_target_pairs={{0,12},{2,14},{4,8},{6,10},{8,4},{10,6},{12,0},{14,2},{1,13},{3,15... | collective-permute-start | bytes 196616 | tf_op jit(solution)/shard_map/ppermute | solution.py:25
  81.5 1.9 %collective-permute-start.19 = (bf16[1,16,2048]{2,1,0:T(8,128)(2,1)S(1)}, bf16[1,16,2048]{2,1,0:T(8,128)(2,1)S(1)}, u32[]{:S(2)}, u32[]{:S(2)}) collective-permute-start(bf16[1,16,2048]{2,1,0:T(8,128)(2,1)S(1)} %get-tuple-element.11), channel_id=1, source_target_pairs={{0,4},{2,6},{4,0},{6,2},{8,12},{10,14},{12,8},{14,10},{1,5},{3,7},... | collective-permute-start | bytes 196616 | tf_op jit(solution)/shard_map/ppermute | solution.py:25
  83.5 2.5 %collective-permute-start.17 = (bf16[1,16,2048]{2,1,0:T(8,128)(2,1)S(1)}, bf16[1,16,2048]{2,1,0:T(8,128)(2,1)S(1)}, u32[]{:S(2)}, u32[]{:S(2)}) collective-permute-start(bf16[1,16,2048]{2,1,0:T(8,128)(2,1)S(1)} %get-tuple-element.9), channel_id=1, source_target_pairs={{0,12},{2,14},{4,8},{6,10},{8,4},{10,6},{12,0},{14,2},{1,13},{3,15... | collective-permute-start | bytes 196616 | tf_op jit(solution)/shard_map/ppermute | solution.py:25
  86.1 1.9 %collective-permute-start.15 = (bf16[1,16,2048]{2,1,0:T(8,128)(2,1)S(1)}, bf16[1,16,2048]{2,1,0:T(8,128)(2,1)S(1)}, u32[]{:S(2)}, u32[]{:S(2)}) collective-permute-start(bf16[1,16,2048]{2,1,0:T(8,128)(2,1)S(1)} %get-tuple-element.8), channel_id=1, source_target_pairs={{0,4},{2,6},{4,0},{6,2},{8,12},{10,14},{12,8},{14,10},{1,5},{3,7},... | collective-permute-start | bytes 196616 | tf_op jit(solution)/shard_map/ppermute | solution.py:25
  88.0 1.6 %collective-permute-done.17 = bf16[1,16,2048]{2,1,0:T(8,128)(2,1)S(1)} collective-permute-done((bf16[1,16,2048]{2,1,0:T(8,128)(2,1)S(1)}, bf16[1,16,2048]{2,1,0:T(8,128)(2,1)S(1)}, u32[]{:S(2)}, u32[]{:S(2)}) %collective-permute-start.17) | collective-permute-done | bytes 65568 | tf_op jit(solution)/shard_map/ppermute | solution.py:25
  89.6 1.6 %collective-permute-done.16 = bf16[1,16,2048]{2,1,0:T(8,128)(2,1)S(1)} collective-permute-done((bf16[1,16,2048]{2,1,0:T(8,128)(2,1)S(1)}, bf16[1,16,2048]{2,1,0:T(8,128)(2,1)S(1)}, u32[]{:S(2)}, u32[]{:S(2)}) %collective-permute-start.16) | collective-permute-done | bytes 65568 | tf_op jit(solution)/shard_map/ppermute | solution.py:25
  91.3 0.7 pad_maximum_fusion.2
  (37 shorter events, 1.0 us)
Async XLA Ops:
  0.6 0.9 copy-start
  3.9 9.4 %collective-permute-start.5 = (bf16[1024,128]{1,0:T(8,128)(2,1)S(1)}, bf16[1024,128]{1,0:T(8,128)(2,1)S(1)}, u32[]{:S(2)}, u32[]{:S(2)}) collective-permute-start(bf16[1024,128]{1,0:T(8,128)(2,1)S(1)} %select_convert_fusion), channel_id=1, source_target_pairs={{0,4},{2,6},{4,0},{6,2},{8,12},{10,14},{12,8},{14,10},{1,5},{3,7},... | collective-permute-start | bytes 786440 | tf_op jit(solution)/shard_map/ppermute | solution.py:25
  9.4 9.2 %collective-permute-start = (bf16[1024,128]{1,0:T(8,128)(2,1)S(1)}, bf16[1024,128]{1,0:T(8,128)(2,1)S(1)}, u32[]{:S(2)}, u32[]{:S(2)}) collective-permute-start(bf16[1024,128]{1,0:T(8,128)(2,1)S(1)} %select_convert_fusion.1), channel_id=1, source_target_pairs={{0,2},{2,0},{4,6},{6,4},{8,10},{10,8},{12,14},{14,12},{1,3},{3,1},... | collective-permute-start | bytes 786440 | tf_op jit(solution)/shard_map/ppermute | solution.py:25
  13.4 6.6 %collective-permute-start.6 = (bf16[512,128]{1,0:T(8,128)(2,1)S(1)}, bf16[512,128]{1,0:T(8,128)(2,1)S(1)}, u32[]{:S(2)}, u32[]{:S(2)}) collective-permute-start(bf16[512,128]{1,0:T(8,128)(2,1)S(1)} %select_convert_fusion.2), channel_id=1, source_target_pairs={{0,2},{2,0},{4,6},{6,4},{8,10},{10,8},{12,14},{14,12},{1,3},{3,1},... | collective-permute-start | bytes 393224 | tf_op jit(solution)/shard_map/ppermute | solution.py:25
  18.8 5.2 %collective-permute-start.1 = (bf16[512,128]{1,0:T(8,128)(2,1)S(1)}, bf16[512,128]{1,0:T(8,128)(2,1)S(1)}, u32[]{:S(2)}, u32[]{:S(2)}) collective-permute-start(bf16[512,128]{1,0:T(8,128)(2,1)S(1)} %select_convert_fusion.3), channel_id=1, source_target_pairs={{0,4},{2,6},{4,0},{6,2},{8,12},{10,14},{12,8},{14,10},{1,5},{3,7},... | collective-permute-start | bytes 393224 | tf_op jit(solution)/shard_map/ppermute | solution.py:25
  20.1 11.6 %collective-permute-start.7 = (bf16[512,128]{1,0:T(8,128)(2,1)S(1)}, bf16[512,128]{1,0:T(8,128)(2,1)S(1)}, u32[]{:S(2)}, u32[]{:S(2)}) collective-permute-start(bf16[512,128]{1,0:T(8,128)(2,1)S(1)} %fusion.27), channel_id=1, source_target_pairs={{0,8},{2,10},{4,12},{6,14},{8,0},{10,2},{12,4},{14,6},{1,9},{3,11}... | collective-permute-start | bytes 393224 | tf_op jit(solution)/shard_map/ppermute | solution.py:25
  24.0 9.6 %collective-permute-start.2 = (bf16[512,128]{1,0:T(8,128)(2,1)S(1)}, bf16[512,128]{1,0:T(8,128)(2,1)S(1)}, u32[]{:S(2)}, u32[]{:S(2)}) collective-permute-start(bf16[512,128]{1,0:T(8,128)(2,1)S(1)} %fusion.26), channel_id=1, source_target_pairs={{0,8},{2,10},{4,12},{6,14},{8,0},{10,2},{12,4},{14,6},{1,9},{3,11}... | collective-permute-start | bytes 393224 | tf_op jit(solution)/shard_map/ppermute | solution.py:25
  31.7 12.2 %copy-start.1 = (bf16[512,4096]{1,0:T(8,128)(2,1)S(1)}, bf16[512,4096]{1,0:T(8,128)(2,1)}, u32[]{:S(2)}) copy-start(bf16[512,4096]{1,0:T(8,128)(2,1)} %slab_ref.1) | copy-start | bytes 12582916
  31.8 5.0 %collective-permute-start.8 = (bf16[512,128]{1,0:T(8,128)(2,1)S(1)}, bf16[512,128]{1,0:T(8,128)(2,1)S(1)}, u32[]{:S(2)}, u32[]{:S(2)}) collective-permute-start(bf16[512,128]{1,0:T(8,128)(2,1)S(1)} %multiply_convert_fusion), channel_id=1, source_target_pairs={{0,2},{2,0},{4,6},{6,4},{8,10},{10,8},{12,14},{14,12},{1,3},{3,1},... | collective-permute-start | bytes 393224 | tf_op jit(solution)/shard_map/ppermute | solution.py:25
  33.6 6.5 %collective-permute-start.3 = (bf16[512,128]{1,0:T(8,128)(2,1)S(1)}, bf16[512,128]{1,0:T(8,128)(2,1)S(1)}, u32[]{:S(2)}, u32[]{:S(2)}) collective-permute-start(bf16[512,128]{1,0:T(8,128)(2,1)S(1)} %multiply_convert_fusion.1), channel_id=1, source_target_pairs={{0,4},{2,6},{4,0},{6,2},{8,12},{10,14},{12,8},{14,10},{1,5},{3,7},... | collective-permute-start | bytes 393224 | tf_op jit(solution)/shard_map/ppermute | solution.py:25
  36.9 6.9 %collective-permute-start.9 = (bf16[1024,128]{1,0:T(8,128)(2,1)S(1)}, bf16[1024,128]{1,0:T(8,128)(2,1)S(1)}, u32[]{:S(2)}, u32[]{:S(2)}) collective-permute-start(bf16[1024,128]{1,0:T(8,128)(2,1)S(1)} %pad_maximum_fusion.1), channel_id=1, source_target_pairs={{0,4},{2,6},{4,0},{6,2},{8,12},{10,14},{12,8},{14,10},{1,5},{3,7},... | collective-permute-start | bytes 786440 | tf_op jit(solution)/shard_map/ppermute | solution.py:25
  40.2 6.4 %collective-permute-start.4 = (bf16[1024,128]{1,0:T(8,128)(2,1)S(1)}, bf16[1024,128]{1,0:T(8,128)(2,1)S(1)}, u32[]{:S(2)}, u32[]{:S(2)}) collective-permute-start(bf16[1024,128]{1,0:T(8,128)(2,1)S(1)} %pad_maximum_fusion), channel_id=1, source_target_pairs={{0,2},{2,0},{4,6},{6,4},{8,10},{10,8},{12,14},{14,12},{1,3},{3,1},... | collective-permute-start | bytes 786440 | tf_op jit(solution)/shard_map/ppermute | solution.py:25
  47.4 1.6 %collective-permute-start.10 = (f32[512,128]{1,0:T(8,128)S(1)}, f32[512,128]{1,0:T(8,128)S(1)}, u32[]{:S(2)}, u32[]{:S(2)}) collective-permute-start(f32[512,128]{1,0:T(8,128)S(1)} %fusion.11.mine_ref), channel_id=1, source_target_pairs={{0,1},{1,0},{2,3},{3,2},{4,5},{5,4},{6,7},{7,6},{8,9},{9,8},{10,11... | collective-permute-start | bytes 786440 | tf_op jit(solution)/shard_map/ppermute | solution.py:25
  49.6 4.3 %collective-permute-start.11 = (f32[128,128]{1,0:T(8,128)S(1)}, f32[128,128]{1,0:T(8,128)S(1)}, u32[]{:S(2)}, u32[]{:S(2)}) collective-permute-start(f32[128,128]{1,0:T(8,128)S(1)} %fusion.22), channel_id=1, source_target_pairs={{0,2},{2,0},{4,6},{6,4},{8,10},{10,8},{12,14},{14,12},{1,3},{3,1},... | collective-permute-start | bytes 196616 | tf_op jit(solution)/shard_map/ppermute | solution.py:25
  54.0 4.3 %collective-permute-start.12 = (f32[128,128]{1,0:T(8,128)S(1)}, f32[128,128]{1,0:T(8,128)S(1)}, u32[]{:S(2)}, u32[]{:S(2)}) collective-permute-start(f32[128,128]{1,0:T(8,128)S(1)} %add.94), channel_id=1, source_target_pairs={{0,4},{2,6},{4,0},{6,2},{8,12},{10,14},{12,8},{14,10},{1,5},{3,7},... | collective-permute-start | bytes 196616 | tf_op jit(solution)/shard_map/ppermute | solution.py:25
  58.3 5.8 %collective-permute-start.13 = (f32[128,128]{1,0:T(8,128)S(1)}, f32[128,128]{1,0:T(8,128)S(1)}, u32[]{:S(2)}, u32[]{:S(2)}) collective-permute-start(f32[128,128]{1,0:T(8,128)S(1)} %add.95), channel_id=1, source_target_pairs={{0,8},{2,10},{4,12},{6,14},{8,0},{10,2},{12,4},{14,6},{1,9},{3,11}... | collective-permute-start | bytes 196616 | tf_op jit(solution)/shard_map/ppermute | solution.py:25
  64.1 2.2 %copy-start.2 = (bf16[512,4096]{1,0:T(8,128)(2,1)S(1)}, bf16[512,4096]{1,0:T(8,128)(2,1)}, u32[]{:S(2)}) copy-start(bf16[512,4096]{1,0:T(8,128)(2,1)} %slab_ref.1) | copy-start | bytes 12582916
  70.9 7.9 %collective-permute-start.18 = (bf16[4,16,2048]{2,1,0:T(8,128)(2,1)S(1)}, bf16[4,16,2048]{2,1,0:T(8,128)(2,1)S(1)}, u32[]{:S(2)}, u32[]{:S(2)}) collective-permute-start(bf16[4,16,2048]{2,1,0:T(8,128)(2,1)S(1)} %fusion.21), channel_id=1, source_target_pairs={{0,2},{2,0},{4,6},{6,4},{8,10},{10,8},{12,14},{14,12},{1,3},{3,1},... | collective-permute-start | bytes 786440 | tf_op jit(solution)/shard_map/ppermute | solution.py:25
  72.5 10.9 %collective-permute-start.14 = (bf16[4,16,2048]{2,1,0:T(8,128)(2,1)S(1)}, bf16[4,16,2048]{2,1,0:T(8,128)(2,1)S(1)}, u32[]{:S(2)}, u32[]{:S(2)}) collective-permute-start(bf16[4,16,2048]{2,1,0:T(8,128)(2,1)S(1)} %fusion.20), channel_id=1, source_target_pairs={{0,2},{2,0},{4,6},{6,4},{8,10},{10,8},{12,14},{14,12},{1,3},{3,1},... | collective-permute-start | bytes 786440 | tf_op jit(solution)/shard_map/ppermute | solution.py:25
  79.0 7.1 %collective-permute-start.21 = (bf16[1,16,2048]{2,1,0:T(8,128)(2,1)S(1)}, bf16[1,16,2048]{2,1,0:T(8,128)(2,1)S(1)}, u32[]{:S(2)}, u32[]{:S(2)}) collective-permute-start(bf16[1,16,2048]{2,1,0:T(8,128)(2,1)S(1)} %get-tuple-element.12), channel_id=1, source_target_pairs={{0,12},{2,14},{4,8},{6,10},{8,4},{10,6},{12,0},{14,2},{1,13},{3,15... | collective-permute-start | bytes 196616 | tf_op jit(solution)/shard_map/ppermute | solution.py:25
  81.5 6.5 %collective-permute-start.20 = (bf16[1,16,2048]{2,1,0:T(8,128)(2,1)S(1)}, bf16[1,16,2048]{2,1,0:T(8,128)(2,1)S(1)}, u32[]{:S(2)}, u32[]{:S(2)}) collective-permute-start(bf16[1,16,2048]{2,1,0:T(8,128)(2,1)S(1)} %get-tuple-element.13), channel_id=1, source_target_pairs={{0,8},{2,10},{4,12},{6,14},{8,0},{10,2},{12,4},{14,6},{1,9},{3,11}... | collective-permute-start | bytes 196616 | tf_op jit(solution)/shard_map/ppermute | solution.py:25
  81.5 6.5 %collective-permute-start.19 = (bf16[1,16,2048]{2,1,0:T(8,128)(2,1)S(1)}, bf16[1,16,2048]{2,1,0:T(8,128)(2,1)S(1)}, u32[]{:S(2)}, u32[]{:S(2)}) collective-permute-start(bf16[1,16,2048]{2,1,0:T(8,128)(2,1)S(1)} %get-tuple-element.11), channel_id=1, source_target_pairs={{0,4},{2,6},{4,0},{6,2},{8,12},{10,14},{12,8},{14,10},{1,5},{3,7},... | collective-permute-start | bytes 196616 | tf_op jit(solution)/shard_map/ppermute | solution.py:25
  83.5 6.1 %collective-permute-start.17 = (bf16[1,16,2048]{2,1,0:T(8,128)(2,1)S(1)}, bf16[1,16,2048]{2,1,0:T(8,128)(2,1)S(1)}, u32[]{:S(2)}, u32[]{:S(2)}) collective-permute-start(bf16[1,16,2048]{2,1,0:T(8,128)(2,1)S(1)} %get-tuple-element.9), channel_id=1, source_target_pairs={{0,12},{2,14},{4,8},{6,10},{8,4},{10,6},{12,0},{14,2},{1,13},{3,15... | collective-permute-start | bytes 196616 | tf_op jit(solution)/shard_map/ppermute | solution.py:25
  86.1 5.2 %collective-permute-start.16 = (bf16[1,16,2048]{2,1,0:T(8,128)(2,1)S(1)}, bf16[1,16,2048]{2,1,0:T(8,128)(2,1)S(1)}, u32[]{:S(2)}, u32[]{:S(2)}) collective-permute-start(bf16[1,16,2048]{2,1,0:T(8,128)(2,1)S(1)} %get-tuple-element.10), channel_id=1, source_target_pairs={{0,8},{2,10},{4,12},{6,14},{8,0},{10,2},{12,4},{14,6},{1,9},{3,11}... | collective-permute-start | bytes 196616 | tf_op jit(solution)/shard_map/ppermute | solution.py:25
  86.1 5.2 %collective-permute-start.15 = (bf16[1,16,2048]{2,1,0:T(8,128)(2,1)S(1)}, bf16[1,16,2048]{2,1,0:T(8,128)(2,1)S(1)}, u32[]{:S(2)}, u32[]{:S(2)}) collective-permute-start(bf16[1,16,2048]{2,1,0:T(8,128)(2,1)S(1)} %get-tuple-element.8), channel_id=1, source_target_pairs={{0,4},{2,6},{4,0},{6,2},{8,12},{10,14},{12,8},{14,10},{1,5},{3,7},... | collective-permute-start | bytes 196616 | tf_op jit(solution)/shard_map/ppermute | solution.py:25

commit v8 on v7

--- a/solution.py
+++ b/solution.py
@@ -8,6 +8,7 @@
 from jax.experimental.pallas import tpu as pltpu
 from jax.sharding import PartitionSpec as P
 
+SKETCH_CHUNKS = 4
 CHUNKS = 2
 
 
@@ -208,7 +209,10 @@
     spans = [slice(c * cols_chunk, (c + 1) * cols_chunk) for c in range(CHUNKS)]
 
     partial_sketch = 0.0
-    for span, order in zip(spans, orders_of("row")):
+    orders = orders_of("row")
+    step = cols_here // SKETCH_CHUNKS
+    for c in range(SKETCH_CHUNKS):
+        span, order = slice(c * step, (c + 1) * step), orders[c % 2]
         local_cols = lax.dot_general(
             activations[:, span],
             start_sketch,

time: 92.2 us -> 89.7 us (0.973)
  waiting for transfers between devices: 44.9 us -> 30.8 us
  starting transfers between devices: 30 us -> 38.9 us
  matrix products: 6.68 us -> 9.12 us
    ppermute x22 -> x32, waiting for transfers between devices: 44.9 us -> 30.8 us  [swap(): return lax.ppermute(value, axis, [(i, i ^ distance) for i in range(size)])]
    ppermute x22 -> x32, starting transfers between devices: 30 us -> 38.9 us  [swap(): return lax.ppermute(value, axis, [(i, i ^ distance) for i in range(size)])]
    dot_general x2 -> x4, matrix products: 4.65 us -> 6.75 us  [per_device(): lax.dot_general(activations[:, span], start_sketch, (((0,), (0,)), ((), (...]
  transfers between devices with their start and end apart: 22 -> 32, of which waited for: 17 -> 19; matrix products, arithmetic and copies ran while one was open for 4% -> 8% of each run, Pallas kernels for 0% -> 0%
where the time goes in v8:
time: 89.7 us; the launch traced here: 89.4 us
  starting transfers between devices  38.9 us (43%)
  waiting for transfers between devices  30.8 us (34%)
  matrix products  9.12 us (10%)
  Pallas kernels  4.43 us (5%)
  local copies, waits for them, and re-layouts  3.34 us (4%)
  other arithmetic  1.83 us (2%)
  between operations  0.99 us (1%)
    ppermute x32, starting transfers between devices, swap(): return lax.ppermute(value, axis, [(i, i ^ distance) for i in range(size)])  38.9 us
    ppermute x32, waiting for transfers between devices, swap(): return lax.ppermute(value, axis, [(i, i ^ distance) for i in range(size)])  30.8 us
    dot_general x4, matrix products, per_device(): lax.dot_general(activations[:, span], start_sketch, (((0,), (0,)), ((), (...  6.75 us
    pallas_call x1, Pallas kernels, make_basis(): pl.pallas_call(functools.partial(basis_kernel, total_cols, root_rows), ou...  4.43 us
    unnamed x6, local copies, waits for them, and re-layouts  3.07 us
  transfers between devices with their start and end apart: 32, of which 19 were waited for; matrix products, arithmetic and copies ran while one was open for 8% of the time, Pallas kernels for 0%

profile of v8, /device:TPU:0, one launch (start us, length us, event | category | flops | bytes accessed | tf_op | source)
XLA Modules:
  0.0 89.4 jit_solution(7890685236786286204)
XLA Ops:
  0.7 0.9 copy-done
  1.5 1.7 %fusion.5 = f32[1024,128]{1,0:T(8,128)S(1)} fusion(bf16[512,128]{1,0:T(8,128)(2,1)S(1)} %copy-done, bf16[512,4096]{1,0:T(8,128)(2,1)} %slab_ref.1), kind=kOutput, calls=%fused_computation.6 | convolution fusion | flops 134217728 | bytes 1703936 | tf_op jit(solution)/shard_map/dot_general | solution.py:216
  3.3 3.1 %collective-permute-start.15 = (bf16[512,128]{1,0:T(8,128)(2,1)S(1)}, bf16[512,128]{1,0:T(8,128)(2,1)S(1)}, u32[]{:S(2)}, u32[]{:S(2)}) collective-permute-start(bf16[512,128]{1,0:T(8,128)(2,1)S(1)} %select_convert_fusion), channel_id=1, source_target_pairs={{0,4},{2,6},{4,0},{6,2},{8,12},{10,14},{12,8},{14,10},{1,5},{3,7},... | collective-permute-start | bytes 393224 | tf_op jit(solution)/shard_map/ppermute | solution.py:26
  6.4 1.7 %fusion.9 = f32[1024,128]{1,0:T(8,128)S(1)} fusion(bf16[512,128]{1,0:T(8,128)(2,1)S(1)} %copy-done, bf16[512,4096]{1,0:T(8,128)(2,1)} %slab_ref.1), kind=kOutput, calls=%fused_computation.10 | convolution fusion | flops 134217728 | bytes 1703936 | tf_op jit(solution)/shard_map/dot_general | solution.py:216
  8.1 1.6 %collective-permute-start.10 = (bf16[512,128]{1,0:T(8,128)(2,1)S(1)}, bf16[512,128]{1,0:T(8,128)(2,1)S(1)}, u32[]{:S(2)}, u32[]{:S(2)}) collective-permute-start(bf16[512,128]{1,0:T(8,128)(2,1)S(1)} %select_convert_fusion.1), channel_id=1, source_target_pairs={{0,2},{2,0},{4,6},{6,4},{8,10},{10,8},{12,14},{14,12},{1,3},{3,1},... | collective-permute-start | bytes 393224 | tf_op jit(solution)/shard_map/ppermute | solution.py:26
  9.6 1.7 %fusion.13 = f32[1024,128]{1,0:T(8,128)S(1)} fusion(bf16[512,128]{1,0:T(8,128)(2,1)S(1)} %copy-done, bf16[512,4096]{1,0:T(8,128)(2,1)} %slab_ref.1), kind=kOutput, calls=%fused_computation.14 | convolution fusion | flops 134217728 | bytes 1703936 | tf_op jit(solution)/shard_map/dot_general | solution.py:216
  11.9 1.7 %fusion.16 = f32[1024,128]{1,0:T(8,128)S(1)} fusion(bf16[512,128]{1,0:T(8,128)(2,1)S(1)} %copy-done, bf16[512,4096]{1,0:T(8,128)(2,1)} %slab_ref.1), kind=kOutput, calls=%fused_computation.17 | convolution fusion | flops 134217728 | bytes 1703936 | tf_op jit(solution)/shard_map/dot_general | solution.py:216
  13.8 2.0 %collective-permute-start.16 = (bf16[256,128]{1,0:T(8,128)(2,1)S(1)}, bf16[256,128]{1,0:T(8,128)(2,1)S(1)}, u32[]{:S(2)}, u32[]{:S(2)}) collective-permute-start(bf16[256,128]{1,0:T(8,128)(2,1)S(1)} %select_convert_fusion.4), channel_id=1, source_target_pairs={{0,2},{2,0},{4,6},{6,4},{8,10},{10,8},{12,14},{14,12},{1,3},{3,1},... | collective-permute-start | bytes 196616 | tf_op jit(solution)/shard_map/ppermute | solution.py:26
  15.9 1.6 %collective-permute-start.11 = (bf16[256,128]{1,0:T(8,128)(2,1)S(1)}, bf16[256,128]{1,0:T(8,128)(2,1)S(1)}, u32[]{:S(2)}, u32[]{:S(2)}) collective-permute-start(bf16[256,128]{1,0:T(8,128)(2,1)S(1)} %select_convert_fusion.5), channel_id=1, source_target_pairs={{0,4},{2,6},{4,0},{6,2},{8,12},{10,14},{12,8},{14,10},{1,5},{3,7},... | collective-permute-start | bytes 196616 | tf_op jit(solution)/shard_map/ppermute | solution.py:26
  17.6 0.6 collective-permute-start.6
  18.2 0.8 collective-permute-done
  19.1 2.0 %collective-permute-start.1 = (bf16[256,128]{1,0:T(8,128)(2,1)S(1)}, bf16[256,128]{1,0:T(8,128)(2,1)S(1)}, u32[]{:S(2)}, u32[]{:S(2)}) collective-permute-start(bf16[256,128]{1,0:T(8,128)(2,1)S(1)} %select_convert_fusion.7), channel_id=1, source_target_pairs={{0,4},{2,6},{4,0},{6,2},{8,12},{10,14},{12,8},{14,10},{1,5},{3,7},... | collective-permute-start | bytes 196616 | tf_op jit(solution)/shard_map/ppermute | solution.py:26
  21.2 2.7 %collective-permute-start.17 = (bf16[256,128]{1,0:T(8,128)(2,1)S(1)}, bf16[256,128]{1,0:T(8,128)(2,1)S(1)}, u32[]{:S(2)}, u32[]{:S(2)}) collective-permute-start(bf16[256,128]{1,0:T(8,128)(2,1)S(1)} %fusion.39), channel_id=1, source_target_pairs={{0,8},{2,10},{4,12},{6,14},{8,0},{10,2},{12,4},{14,6},{1,9},{3,11}... | collective-permute-start | bytes 196616 | tf_op jit(solution)/shard_map/ppermute | solution.py:26
  24.3 2.7 %collective-permute-start.7 = (bf16[256,128]{1,0:T(8,128)(2,1)S(1)}, bf16[256,128]{1,0:T(8,128)(2,1)S(1)}, u32[]{:S(2)}, u32[]{:S(2)}) collective-permute-start(bf16[256,128]{1,0:T(8,128)(2,1)S(1)} %fusion.37), channel_id=1, source_target_pairs={{0,8},{2,10},{4,12},{6,14},{8,0},{10,2},{12,4},{14,6},{1,9},{3,11}... | collective-permute-start | bytes 196616 | tf_op jit(solution)/shard_map/ppermute | solution.py:26
  27.4 3.3 %collective-permute-done.17 = bf16[256,128]{1,0:T(8,128)(2,1)S(1)} collective-permute-done((bf16[256,128]{1,0:T(8,128)(2,1)S(1)}, bf16[256,128]{1,0:T(8,128)(2,1)S(1)}, u32[]{:S(2)}, u32[]{:S(2)}) %collective-permute-start.17) | collective-permute-done | bytes 65568 | tf_op jit(solution)/shard_map/ppermute | solution.py:26
  30.7 0.6 collective-permute-start.18
  31.9 1.1 %collective-permute-done.7 = bf16[256,128]{1,0:T(8,128)(2,1)S(1)} collective-permute-done((bf16[256,128]{1,0:T(8,128)(2,1)S(1)}, bf16[256,128]{1,0:T(8,128)(2,1)S(1)}, u32[]{:S(2)}, u32[]{:S(2)}) %collective-permute-start.7) | collective-permute-done | bytes 65568 | tf_op jit(solution)/shard_map/ppermute | solution.py:26
  33.1 0.6 collective-permute-start.8
  33.8 1.4 %collective-permute-start.3 = (bf16[256,128]{1,0:T(8,128)(2,1)S(1)}, bf16[256,128]{1,0:T(8,128)(2,1)S(1)}, u32[]{:S(2)}, u32[]{:S(2)}) collective-permute-start(bf16[256,128]{1,0:T(8,128)(2,1)S(1)} %multiply_convert_fusion.3), channel_id=1, source_target_pairs={{0,4},{2,6},{4,0},{6,2},{8,12},{10,14},{12,8},{14,10},{1,5},{3,7},... | collective-permute-start | bytes 196616 | tf_op jit(solution)/shard_map/ppermute | solution.py:26
  35.2 0.7 collective-permute-start.19
  36.0 0.8 collective-permute-done.13
  36.8 0.7 collective-permute-start.14
  37.5 0.5 collective-permute-done.8
  38.1 0.5 collective-permute-start.9
  38.9 0.8 collective-permute-start.4
  39.7 0.6 collective-permute-done.19
  40.8 1.0 %collective-permute-done.14 = bf16[512,128]{1,0:T(8,128)(2,1)S(1)} collective-permute-done((bf16[512,128]{1,0:T(8,128)(2,1)S(1)}, bf16[512,128]{1,0:T(8,128)(2,1)S(1)}, u32[]{:S(2)}, u32[]{:S(2)}) %collective-permute-start.14) | collective-permute-done | bytes 131104 | tf_op jit(solution)/shard_map/ppermute | solution.py:26
  42.3 0.8 collective-permute-done.9
  44.5 1.5 %collective-permute-done.20.other_ref = f32[512,128]{1,0:T(8,128)S(1)} collective-permute-done((f32[512,128]{1,0:T(8,128)S(1)}, f32[512,128]{1,0:T(8,128)S(1)}, u32[]{:S(2)}, u32[]{:S(2)}) %collective-permute-start.20) | collective-permute-done | bytes 262176 | tf_op jit(solution)/shard_map/ppermute | solution.py:26
  46.0 0.6 fusion.32
  46.7 0.8 collective-permute-start.21
  47.5 3.5 %collective-permute-done.21 = f32[128,128]{1,0:T(8,128)S(1)} collective-permute-done((f32[128,128]{1,0:T(8,128)S(1)}, f32[128,128]{1,0:T(8,128)S(1)}, u32[]{:S(2)}, u32[]{:S(2)}) %collective-permute-start.21) | collective-permute-done | bytes 65568 | tf_op jit(solution)/shard_map/ppermute | solution.py:26
  51.0 1.4 %collective-permute-start.22 = (f32[128,128]{1,0:T(8,128)S(1)}, f32[128,128]{1,0:T(8,128)S(1)}, u32[]{:S(2)}, u32[]{:S(2)}) collective-permute-start(f32[128,128]{1,0:T(8,128)S(1)} %add.128), channel_id=1, source_target_pairs={{0,4},{2,6},{4,0},{6,2},{8,12},{10,14},{12,8},{14,10},{1,5},{3,7},... | collective-permute-start | bytes 196616 | tf_op jit(solution)/shard_map/ppermute | solution.py:26
  52.4 3.0 %collective-permute-done.22 = f32[128,128]{1,0:T(8,128)S(1)} collective-permute-done((f32[128,128]{1,0:T(8,128)S(1)}, f32[128,128]{1,0:T(8,128)S(1)}, u32[]{:S(2)}, u32[]{:S(2)}) %collective-permute-start.22) | collective-permute-done | bytes 65568 | tf_op jit(solution)/shard_map/ppermute | solution.py:26
  55.3 2.2 %collective-permute-start.23 = (f32[128,128]{1,0:T(8,128)S(1)}, f32[128,128]{1,0:T(8,128)S(1)}, u32[]{:S(2)}, u32[]{:S(2)}) collective-permute-start(f32[128,128]{1,0:T(8,128)S(1)} %add.129), channel_id=1, source_target_pairs={{0,8},{2,10},{4,12},{6,14},{8,0},{10,2},{12,4},{14,6},{1,9},{3,11}... | collective-permute-start | bytes 196616 | tf_op jit(solution)/shard_map/ppermute | solution.py:26
  57.6 3.0 %collective-permute-done.23 = f32[128,128]{1,0:T(8,128)S(1)} collective-permute-done((f32[128,128]{1,0:T(8,128)S(1)}, f32[128,128]{1,0:T(8,128)S(1)}, u32[]{:S(2)}, u32[]{:S(2)}) %collective-permute-start.23) | collective-permute-done | bytes 65568 | tf_op jit(solution)/shard_map/ppermute | solution.py:26
  60.6 2.2 %copy-done.2 = bf16[512,4096]{1,0:T(8,128)(2,1)S(1)} copy-done((bf16[512,4096]{1,0:T(8,128)(2,1)S(1)}, bf16[512,4096]{1,0:T(8,128)(2,1)}, u32[]{:S(2)}) %copy-start.2) | copy-done | bytes 4194328
  62.8 4.4 %make_basis.1 = (f32[512,128]{1,0:T(8,128)}, f32[128,4096]{1,0:T(8,128)S(1)}) custom-call(f32[128,128]{1,0:T(8,128)S(1)} %add.130.gram_ref, f32[512,128]{1,0:T(8,128)S(1)} %fusion.2.mine_ref, f32[512,128]{1,0:T(8,128)S(1)} %collective-permute-done.20.other_ref, bf16[512,4096]{1,0:T(8,128)(2,1)S(1)} %copy-done.2), custom_call_target="tpu_custom_call" | custom-call | tf_op jit(solution)/shard_map/make_basis/pallas_call | solution.py:183
  67.4 0.8 collective-permute-start.28
  68.3 1.3 %collective-permute-start.24 = (bf16[4,16,2048]{2,1,0:T(8,128)(2,1)S(1)}, bf16[4,16,2048]{2,1,0:T(8,128)(2,1)S(1)}, u32[]{:S(2)}, u32[]{:S(2)}) collective-permute-start(bf16[4,16,2048]{2,1,0:T(8,128)(2,1)S(1)} %fusion.18), channel_id=1, source_target_pairs={{0,2},{2,0},{4,6},{6,4},{8,10},{10,8},{12,14},{14,12},{1,3},{3,1},... | collective-permute-start | bytes 786440 | tf_op jit(solution)/shard_map/ppermute | solution.py:26
  69.6 5.6 %collective-permute-done.28 = bf16[4,16,2048]{2,1,0:T(8,128)(2,1)S(1)} collective-permute-done((bf16[4,16,2048]{2,1,0:T(8,128)(2,1)S(1)}, bf16[4,16,2048]{2,1,0:T(8,128)(2,1)S(1)}, u32[]{:S(2)}, u32[]{:S(2)}) %collective-permute-start.28) | collective-permute-done | bytes 262176 | tf_op jit(solution)/shard_map/ppermute | solution.py:26
  75.3 3.6 %collective-permute-start.31 = (bf16[1,16,2048]{2,1,0:T(8,128)(2,1)S(1)}, bf16[1,16,2048]{2,1,0:T(8,128)(2,1)S(1)}, u32[]{:S(2)}, u32[]{:S(2)}) collective-permute-start(bf16[1,16,2048]{2,1,0:T(8,128)(2,1)S(1)} %get-tuple-element.12), channel_id=1, source_target_pairs={{0,12},{2,14},{4,8},{6,10},{8,4},{10,6},{12,0},{14,2},{1,13},{3,15... | collective-permute-start | bytes 196616 | tf_op jit(solution)/shard_map/ppermute | solution.py:26
  78.9 0.9 collective-permute-start.29
  79.8 3.6 %collective-permute-start.27 = (bf16[1,16,2048]{2,1,0:T(8,128)(2,1)S(1)}, bf16[1,16,2048]{2,1,0:T(8,128)(2,1)S(1)}, u32[]{:S(2)}, u32[]{:S(2)}) collective-permute-start(bf16[1,16,2048]{2,1,0:T(8,128)(2,1)S(1)} %get-tuple-element.9), channel_id=1, source_target_pairs={{0,12},{2,14},{4,8},{6,10},{8,4},{10,6},{12,0},{14,2},{1,13},{3,15... | collective-permute-start | bytes 196616 | tf_op jit(solution)/shard_map/ppermute | solution.py:26
  83.4 0.9 collective-permute-start.25
  84.3 1.9 %collective-permute-done.27 = bf16[1,16,2048]{2,1,0:T(8,128)(2,1)S(1)} collective-permute-done((bf16[1,16,2048]{2,1,0:T(8,128)(2,1)S(1)}, bf16[1,16,2048]{2,1,0:T(8,128)(2,1)S(1)}, u32[]{:S(2)}, u32[]{:S(2)}) %collective-permute-start.27) | collective-permute-done | bytes 65568 | tf_op jit(solution)/shard_map/ppermute | solution.py:26
  86.2 2.4 %collective-permute-done.26 = bf16[1,16,2048]{2,1,0:T(8,128)(2,1)S(1)} collective-permute-done((bf16[1,16,2048]{2,1,0:T(8,128)(2,1)S(1)}, bf16[1,16,2048]{2,1,0:T(8,128)(2,1)S(1)}, u32[]{:S(2)}, u32[]{:S(2)}) %collective-permute-start.26) | collective-permute-done | bytes 65568 | tf_op jit(solution)/shard_map/ppermute | solution.py:26
  88.6 0.7 pad_maximum_fusion
  (77 shorter events, 5.9 us)
Async XLA Ops:
  0.6 0.9 %copy-start = (bf16[512,128]{1,0:T(8,128)(2,1)S(1)}, bf16[512,128]{1,0:T(8,128)(2,1)}, u32[]{:S(2)}) copy-start(bf16[512,128]{1,0:T(8,128)(2,1)} %param.3) | copy-start | bytes 393220
  3.3 10.5 %collective-permute-start.15 = (bf16[512,128]{1,0:T(8,128)(2,1)S(1)}, bf16[512,128]{1,0:T(8,128)(2,1)S(1)}, u32[]{:S(2)}, u32[]{:S(2)}) collective-permute-start(bf16[512,128]{1,0:T(8,128)(2,1)S(1)} %select_convert_fusion), channel_id=1, source_target_pairs={{0,4},{2,6},{4,0},{6,2},{8,12},{10,14},{12,8},{14,10},{1,5},{3,7},... | collective-permute-start | bytes 393224 | tf_op jit(solution)/shard_map/ppermute | solution.py:26
  8.1 7.8 %collective-permute-start.10 = (bf16[512,128]{1,0:T(8,128)(2,1)S(1)}, bf16[512,128]{1,0:T(8,128)(2,1)S(1)}, u32[]{:S(2)}, u32[]{:S(2)}) collective-permute-start(bf16[512,128]{1,0:T(8,128)(2,1)S(1)} %select_convert_fusion.1), channel_id=1, source_target_pairs={{0,2},{2,0},{4,6},{6,4},{8,10},{10,8},{12,14},{14,12},{1,3},{3,1},... | collective-permute-start | bytes 393224 | tf_op jit(solution)/shard_map/ppermute | solution.py:26
  11.4 6.2 %collective-permute-start.5 = (bf16[512,128]{1,0:T(8,128)(2,1)S(1)}, bf16[512,128]{1,0:T(8,128)(2,1)S(1)}, u32[]{:S(2)}, u32[]{:S(2)}) collective-permute-start(bf16[512,128]{1,0:T(8,128)(2,1)S(1)} %select_convert_fusion.2), channel_id=1, source_target_pairs={{0,4},{2,6},{4,0},{6,2},{8,12},{10,14},{12,8},{14,10},{1,5},{3,7},... | collective-permute-start | bytes 393224 | tf_op jit(solution)/shard_map/ppermute | solution.py:26
  13.6 5.5 %collective-permute-start = (bf16[512,128]{1,0:T(8,128)(2,1)S(1)}, bf16[512,128]{1,0:T(8,128)(2,1)S(1)}, u32[]{:S(2)}, u32[]{:S(2)}) collective-permute-start(bf16[512,128]{1,0:T(8,128)(2,1)S(1)} %select_convert_fusion.3), channel_id=1, source_target_pairs={{0,2},{2,0},{4,6},{6,4},{8,10},{10,8},{12,14},{14,12},{1,3},{3,1},... | collective-permute-start | bytes 393224 | tf_op jit(solution)/shard_map/ppermute | solution.py:26
  13.8 7.3 %collective-permute-start.16 = (bf16[256,128]{1,0:T(8,128)(2,1)S(1)}, bf16[256,128]{1,0:T(8,128)(2,1)S(1)}, u32[]{:S(2)}, u32[]{:S(2)}) collective-permute-start(bf16[256,128]{1,0:T(8,128)(2,1)S(1)} %select_convert_fusion.4), channel_id=1, source_target_pairs={{0,2},{2,0},{4,6},{6,4},{8,10},{10,8},{12,14},{14,12},{1,3},{3,1},... | collective-permute-start | bytes 196616 | tf_op jit(solution)/shard_map/ppermute | solution.py:26
  15.9 24.5 %copy-start.1 = (bf16[512,4096]{1,0:T(8,128)(2,1)S(1)}, bf16[512,4096]{1,0:T(8,128)(2,1)}, u32[]{:S(2)}) copy-start(bf16[512,4096]{1,0:T(8,128)(2,1)} %slab_ref.1) | copy-start | bytes 12582916
  15.9 8.0 %collective-permute-start.11 = (bf16[256,128]{1,0:T(8,128)(2,1)S(1)}, bf16[256,128]{1,0:T(8,128)(2,1)S(1)}, u32[]{:S(2)}, u32[]{:S(2)}) collective-permute-start(bf16[256,128]{1,0:T(8,128)(2,1)S(1)} %select_convert_fusion.5), channel_id=1, source_target_pairs={{0,4},{2,6},{4,0},{6,2},{8,12},{10,14},{12,8},{14,10},{1,5},{3,7},... | collective-permute-start | bytes 196616 | tf_op jit(solution)/shard_map/ppermute | solution.py:26
  17.6 6.7 %collective-permute-start.6 = (bf16[256,128]{1,0:T(8,128)(2,1)S(1)}, bf16[256,128]{1,0:T(8,128)(2,1)S(1)}, u32[]{:S(2)}, u32[]{:S(2)}) collective-permute-start(bf16[256,128]{1,0:T(8,128)(2,1)S(1)} %select_convert_fusion.6), channel_id=1, source_target_pairs={{0,2},{2,0},{4,6},{6,4},{8,10},{10,8},{12,14},{14,12},{1,3},{3,1},... | collective-permute-start | bytes 196616 | tf_op jit(solution)/shard_map/ppermute | solution.py:26
  19.1 7.9 %collective-permute-start.1 = (bf16[256,128]{1,0:T(8,128)(2,1)S(1)}, bf16[256,128]{1,0:T(8,128)(2,1)S(1)}, u32[]{:S(2)}, u32[]{:S(2)}) collective-permute-start(bf16[256,128]{1,0:T(8,128)(2,1)S(1)} %select_convert_fusion.7), channel_id=1, source_target_pairs={{0,4},{2,6},{4,0},{6,2},{8,12},{10,14},{12,8},{14,10},{1,5},{3,7},... | collective-permute-start | bytes 196616 | tf_op jit(solution)/shard_map/ppermute | solution.py:26
  21.2 9.5 %collective-permute-start.17 = (bf16[256,128]{1,0:T(8,128)(2,1)S(1)}, bf16[256,128]{1,0:T(8,128)(2,1)S(1)}, u32[]{:S(2)}, u32[]{:S(2)}) collective-permute-start(bf16[256,128]{1,0:T(8,128)(2,1)S(1)} %fusion.39), channel_id=1, source_target_pairs={{0,8},{2,10},{4,12},{6,14},{8,0},{10,2},{12,4},{14,6},{1,9},{3,11}... | collective-permute-start | bytes 196616 | tf_op jit(solution)/shard_map/ppermute | solution.py:26
  23.9 7.7 %collective-permute-start.12 = (bf16[256,128]{1,0:T(8,128)(2,1)S(1)}, bf16[256,128]{1,0:T(8,128)(2,1)S(1)}, u32[]{:S(2)}, u32[]{:S(2)}) collective-permute-start(bf16[256,128]{1,0:T(8,128)(2,1)S(1)} %fusion.38), channel_id=1, source_target_pairs={{0,8},{2,10},{4,12},{6,14},{8,0},{10,2},{12,4},{14,6},{1,9},{3,11}... | collective-permute-start | bytes 196616 | tf_op jit(solution)/shard_map/ppermute | solution.py:26
  24.3 8.7 %collective-permute-start.7 = (bf16[256,128]{1,0:T(8,128)(2,1)S(1)}, bf16[256,128]{1,0:T(8,128)(2,1)S(1)}, u32[]{:S(2)}, u32[]{:S(2)}) collective-permute-start(bf16[256,128]{1,0:T(8,128)(2,1)S(1)} %fusion.37), channel_id=1, source_target_pairs={{0,8},{2,10},{4,12},{6,14},{8,0},{10,2},{12,4},{14,6},{1,9},{3,11}... | collective-permute-start | bytes 196616 | tf_op jit(solution)/shard_map/ppermute | solution.py:26
  27.0 6.7 %collective-permute-start.2 = (bf16[256,128]{1,0:T(8,128)(2,1)S(1)}, bf16[256,128]{1,0:T(8,128)(2,1)S(1)}, u32[]{:S(2)}, u32[]{:S(2)}) collective-permute-start(bf16[256,128]{1,0:T(8,128)(2,1)S(1)} %fusion.36), channel_id=1, source_target_pairs={{0,8},{2,10},{4,12},{6,14},{8,0},{10,2},{12,4},{14,6},{1,9},{3,11}... | collective-permute-start | bytes 196616 | tf_op jit(solution)/shard_map/ppermute | solution.py:26
  30.7 4.5 %collective-permute-start.18 = (bf16[256,128]{1,0:T(8,128)(2,1)S(1)}, bf16[256,128]{1,0:T(8,128)(2,1)S(1)}, u32[]{:S(2)}, u32[]{:S(2)}) collective-permute-start(bf16[256,128]{1,0:T(8,128)(2,1)S(1)} %multiply_convert_fusion), channel_id=1, source_target_pairs={{0,2},{2,0},{4,6},{6,4},{8,10},{10,8},{12,14},{14,12},{1,3},{3,1},... | collective-permute-start | bytes 196616 | tf_op jit(solution)/shard_map/ppermute | solution.py:26
  31.7 5.1 %collective-permute-start.13 = (bf16[256,128]{1,0:T(8,128)(2,1)S(1)}, bf16[256,128]{1,0:T(8,128)(2,1)S(1)}, u32[]{:S(2)}, u32[]{:S(2)}) collective-permute-start(bf16[256,128]{1,0:T(8,128)(2,1)S(1)} %multiply_convert_fusion.1), channel_id=1, source_target_pairs={{0,4},{2,6},{4,0},{6,2},{8,12},{10,14},{12,8},{14,10},{1,5},{3,7},... | collective-permute-start | bytes 196616 | tf_op jit(solution)/shard_map/ppermute | solution.py:26
  33.1 5.0 %collective-permute-start.8 = (bf16[256,128]{1,0:T(8,128)(2,1)S(1)}, bf16[256,128]{1,0:T(8,128)(2,1)S(1)}, u32[]{:S(2)}, u32[]{:S(2)}) collective-permute-start(bf16[256,128]{1,0:T(8,128)(2,1)S(1)} %multiply_convert_fusion.2), channel_id=1, source_target_pairs={{0,2},{2,0},{4,6},{6,4},{8,10},{10,8},{12,14},{14,12},{1,3},{3,1},... | collective-permute-start | bytes 196616 | tf_op jit(solution)/shard_map/ppermute | solution.py:26
  33.8 5.1 %collective-permute-start.3 = (bf16[256,128]{1,0:T(8,128)(2,1)S(1)}, bf16[256,128]{1,0:T(8,128)(2,1)S(1)}, u32[]{:S(2)}, u32[]{:S(2)}) collective-permute-start(bf16[256,128]{1,0:T(8,128)(2,1)S(1)} %multiply_convert_fusion.3), channel_id=1, source_target_pairs={{0,4},{2,6},{4,0},{6,2},{8,12},{10,14},{12,8},{14,10},{1,5},{3,7},... | collective-permute-start | bytes 196616 | tf_op jit(solution)/shard_map/ppermute | solution.py:26
  35.2 5.0 %collective-permute-start.19 = (bf16[512,128]{1,0:T(8,128)(2,1)S(1)}, bf16[512,128]{1,0:T(8,128)(2,1)S(1)}, u32[]{:S(2)}, u32[]{:S(2)}) collective-permute-start(bf16[512,128]{1,0:T(8,128)(2,1)S(1)} %pad_maximum_fusion.4), channel_id=1, source_target_pairs={{0,4},{2,6},{4,0},{6,2},{8,12},{10,14},{12,8},{14,10},{1,5},{3,7},... | collective-permute-start | bytes 393224 | tf_op jit(solution)/shard_map/ppermute | solution.py:26
  36.8 5.0 %collective-permute-start.14 = (bf16[512,128]{1,0:T(8,128)(2,1)S(1)}, bf16[512,128]{1,0:T(8,128)(2,1)S(1)}, u32[]{:S(2)}, u32[]{:S(2)}) collective-permute-start(bf16[512,128]{1,0:T(8,128)(2,1)S(1)} %pad_maximum_fusion.3), channel_id=1, source_target_pairs={{0,2},{2,0},{4,6},{6,4},{8,10},{10,8},{12,14},{14,12},{1,3},{3,1},... | collective-permute-start | bytes 393224 | tf_op jit(solution)/shard_map/ppermute | solution.py:26
  38.1 5.0 %collective-permute-start.9 = (bf16[512,128]{1,0:T(8,128)(2,1)S(1)}, bf16[512,128]{1,0:T(8,128)(2,1)S(1)}, u32[]{:S(2)}, u32[]{:S(2)}) collective-permute-start(bf16[512,128]{1,0:T(8,128)(2,1)S(1)} %pad_maximum_fusion.2), channel_id=1, source_target_pairs={{0,4},{2,6},{4,0},{6,2},{8,12},{10,14},{12,8},{14,10},{1,5},{3,7},... | collective-permute-start | bytes 393224 | tf_op jit(solution)/shard_map/ppermute | solution.py:26
  38.9 5.0 %collective-permute-start.4 = (bf16[512,128]{1,0:T(8,128)(2,1)S(1)}, bf16[512,128]{1,0:T(8,128)(2,1)S(1)}, u32[]{:S(2)}, u32[]{:S(2)}) collective-permute-start(bf16[512,128]{1,0:T(8,128)(2,1)S(1)} %pad_maximum_fusion.1), channel_id=1, source_target_pairs={{0,2},{2,0},{4,6},{6,4},{8,10},{10,8},{12,14},{14,12},{1,3},{3,1},... | collective-permute-start | bytes 393224 | tf_op jit(solution)/shard_map/ppermute | solution.py:26
  44.4 1.6 %collective-permute-start.20 = (f32[512,128]{1,0:T(8,128)S(1)}, f32[512,128]{1,0:T(8,128)S(1)}, u32[]{:S(2)}, u32[]{:S(2)}) collective-permute-start(f32[512,128]{1,0:T(8,128)S(1)} %fusion.2.mine_ref), channel_id=1, source_target_pairs={{0,1},{1,0},{2,3},{3,2},{4,5},{5,4},{6,7},{7,6},{8,9},{9,8},{10,11... | collective-permute-start | bytes 786440 | tf_op jit(solution)/shard_map/ppermute | solution.py:26
  46.7 4.3 %collective-permute-start.21 = (f32[128,128]{1,0:T(8,128)S(1)}, f32[128,128]{1,0:T(8,128)S(1)}, u32[]{:S(2)}, u32[]{:S(2)}) collective-permute-start(f32[128,128]{1,0:T(8,128)S(1)} %fusion.32), channel_id=1, source_target_pairs={{0,2},{2,0},{4,6},{6,4},{8,10},{10,8},{12,14},{14,12},{1,3},{3,1},... | collective-permute-start | bytes 196616 | tf_op jit(solution)/shard_map/ppermute | solution.py:26
  51.0 4.3 %collective-permute-start.22 = (f32[128,128]{1,0:T(8,128)S(1)}, f32[128,128]{1,0:T(8,128)S(1)}, u32[]{:S(2)}, u32[]{:S(2)}) collective-permute-start(f32[128,128]{1,0:T(8,128)S(1)} %add.128), channel_id=1, source_target_pairs={{0,4},{2,6},{4,0},{6,2},{8,12},{10,14},{12,8},{14,10},{1,5},{3,7},... | collective-permute-start | bytes 196616 | tf_op jit(solution)/shard_map/ppermute | solution.py:26
  55.3 5.2 %collective-permute-start.23 = (f32[128,128]{1,0:T(8,128)S(1)}, f32[128,128]{1,0:T(8,128)S(1)}, u32[]{:S(2)}, u32[]{:S(2)}) collective-permute-start(f32[128,128]{1,0:T(8,128)S(1)} %add.129), channel_id=1, source_target_pairs={{0,8},{2,10},{4,12},{6,14},{8,0},{10,2},{12,4},{14,6},{1,9},{3,11}... | collective-permute-start | bytes 196616 | tf_op jit(solution)/shard_map/ppermute | solution.py:26
  60.6 2.2 %copy-start.2 = (bf16[512,4096]{1,0:T(8,128)(2,1)S(1)}, bf16[512,4096]{1,0:T(8,128)(2,1)}, u32[]{:S(2)}) copy-start(bf16[512,4096]{1,0:T(8,128)(2,1)} %slab_ref.1) | copy-start | bytes 12582916
  67.4 7.8 %collective-permute-start.28 = (bf16[4,16,2048]{2,1,0:T(8,128)(2,1)S(1)}, bf16[4,16,2048]{2,1,0:T(8,128)(2,1)S(1)}, u32[]{:S(2)}, u32[]{:S(2)}) collective-permute-start(bf16[4,16,2048]{2,1,0:T(8,128)(2,1)S(1)} %fusion.19), channel_id=1, source_target_pairs={{0,2},{2,0},{4,6},{6,4},{8,10},{10,8},{12,14},{14,12},{1,3},{3,1},... | collective-permute-start | bytes 786440 | tf_op jit(solution)/shard_map/ppermute | solution.py:26
  68.3 11.4 %collective-permute-start.24 = (bf16[4,16,2048]{2,1,0:T(8,128)(2,1)S(1)}, bf16[4,16,2048]{2,1,0:T(8,128)(2,1)S(1)}, u32[]{:S(2)}, u32[]{:S(2)}) collective-permute-start(bf16[4,16,2048]{2,1,0:T(8,128)(2,1)S(1)} %fusion.18), channel_id=1, source_target_pairs={{0,2},{2,0},{4,6},{6,4},{8,10},{10,8},{12,14},{14,12},{1,3},{3,1},... | collective-permute-start | bytes 786440 | tf_op jit(solution)/shard_map/ppermute | solution.py:26
  75.3 8.2 %collective-permute-start.31 = (bf16[1,16,2048]{2,1,0:T(8,128)(2,1)S(1)}, bf16[1,16,2048]{2,1,0:T(8,128)(2,1)S(1)}, u32[]{:S(2)}, u32[]{:S(2)}) collective-permute-start(bf16[1,16,2048]{2,1,0:T(8,128)(2,1)S(1)} %get-tuple-element.12), channel_id=1, source_target_pairs={{0,12},{2,14},{4,8},{6,10},{8,4},{10,6},{12,0},{14,2},{1,13},{3,15... | collective-permute-start | bytes 196616 | tf_op jit(solution)/shard_map/ppermute | solution.py:26
  78.9 5.4 %collective-permute-start.30 = (bf16[1,16,2048]{2,1,0:T(8,128)(2,1)S(1)}, bf16[1,16,2048]{2,1,0:T(8,128)(2,1)S(1)}, u32[]{:S(2)}, u32[]{:S(2)}) collective-permute-start(bf16[1,16,2048]{2,1,0:T(8,128)(2,1)S(1)} %get-tuple-element.13), channel_id=1, source_target_pairs={{0,8},{2,10},{4,12},{6,14},{8,0},{10,2},{12,4},{14,6},{1,9},{3,11}... | collective-permute-start | bytes 196616 | tf_op jit(solution)/shard_map/ppermute | solution.py:26
  78.9 5.4 %collective-permute-start.29 = (bf16[1,16,2048]{2,1,0:T(8,128)(2,1)S(1)}, bf16[1,16,2048]{2,1,0:T(8,128)(2,1)S(1)}, u32[]{:S(2)}, u32[]{:S(2)}) collective-permute-start(bf16[1,16,2048]{2,1,0:T(8,128)(2,1)S(1)} %get-tuple-element.11), channel_id=1, source_target_pairs={{0,4},{2,6},{4,0},{6,2},{8,12},{10,14},{12,8},{14,10},{1,5},{3,7},... | collective-permute-start | bytes 196616 | tf_op jit(solution)/shard_map/ppermute | solution.py:26
  79.8 6.4 %collective-permute-start.27 = (bf16[1,16,2048]{2,1,0:T(8,128)(2,1)S(1)}, bf16[1,16,2048]{2,1,0:T(8,128)(2,1)S(1)}, u32[]{:S(2)}, u32[]{:S(2)}) collective-permute-start(bf16[1,16,2048]{2,1,0:T(8,128)(2,1)S(1)} %get-tuple-element.9), channel_id=1, source_target_pairs={{0,12},{2,14},{4,8},{6,10},{8,4},{10,6},{12,0},{14,2},{1,13},{3,15... | collective-permute-start | bytes 196616 | tf_op jit(solution)/shard_map/ppermute | solution.py:26
  83.4 5.2 %collective-permute-start.26 = (bf16[1,16,2048]{2,1,0:T(8,128)(2,1)S(1)}, bf16[1,16,2048]{2,1,0:T(8,128)(2,1)S(1)}, u32[]{:S(2)}, u32[]{:S(2)}) collective-permute-start(bf16[1,16,2048]{2,1,0:T(8,128)(2,1)S(1)} %get-tuple-element.10), channel_id=1, source_target_pairs={{0,8},{2,10},{4,12},{6,14},{8,0},{10,2},{12,4},{14,6},{1,9},{3,11}... | collective-permute-start | bytes 196616 | tf_op jit(solution)/shard_map/ppermute | solution.py:26
  83.4 5.2 %collective-permute-start.25 = (bf16[1,16,2048]{2,1,0:T(8,128)(2,1)S(1)}, bf16[1,16,2048]{2,1,0:T(8,128)(2,1)S(1)}, u32[]{:S(2)}, u32[]{:S(2)}) collective-permute-start(bf16[1,16,2048]{2,1,0:T(8,128)(2,1)S(1)} %get-tuple-element.8), channel_id=1, source_target_pairs={{0,4},{2,6},{4,0},{6,2},{8,12},{10,14},{12,8},{14,10},{1,5},{3,7},... | collective-permute-start | bytes 196616 | tf_op jit(solution)/shard_map/ppermute | solution.py:26

commit v9 on v8

--- a/solution.py
+++ b/solution.py
@@ -10,6 +10,8 @@
 
 SKETCH_CHUNKS = 4
 CHUNKS = 2
+TILE = 512
+KERNEL_VMEM = 50 * 2**20
 
 
 def levels_of(size):
@@ -62,8 +64,8 @@
 def sum_and_share(value, axis, order, scale):
     for bit in order[:-1]:
         upper = bit_of(axis, bit) == 1
-        half = value.shape[0] // 2
-        low, high = value[:half], value[half:]
+        half = value.shape[1] // 2
+        low, high = value[:, :half], value[:, half:]
         send = jnp.where(upper, low, high).astype(jnp.bfloat16)
         landed = swap(send, axis, 1 << bit)
         value = jnp.where(upper, high, low) + landed.astype(jnp.float32)
@@ -73,7 +75,7 @@
         upper = bit_of(axis, bit) == 1
         other = swap(block, axis, 1 << bit)
         block = jnp.concatenate(
-            [jnp.where(upper, other, block), jnp.where(upper, block, other)], axis=0
+            [jnp.where(upper, other, block), jnp.where(upper, block, other)], axis=1
         )
     return block
 
@@ -83,6 +85,55 @@
     if len(bits) < 3:
         return [bits, bits]
     return [bits, [bits[1], bits[0]] + bits[2:]]
+
+
+def fetch_tiles(slab_ref, buffer, arrived):
+    copies = []
+    for tile in range(buffer.shape[0]):
+        span = pl.ds(tile * TILE, TILE)
+        copies.append(
+            pltpu.make_async_copy(slab_ref.at[:, span], buffer.at[tile], arrived.at[tile])
+        )
+    for copy in copies:
+        copy.start()
+    return copies
+
+
+def sketch_kernel(start_ref, slab_ref, *refs):
+    outs, (start_buffer, buffer, start_here, arrived) = refs[:-4], refs[-4:]
+    start = pltpu.make_async_copy(start_ref, start_buffer, start_here)
+    start.start()
+    copies = fetch_tiles(slab_ref, buffer, arrived)
+    start.wait()
+    left = start_buffer[...].T
+    for tile, copy in enumerate(copies):
+        copy.wait()
+        out, inner = divmod(tile * TILE, outs[0].shape[1])
+        outs[out][:, inner : inner + TILE] = lax.dot_general(
+            left, buffer[tile], (((1,), (0,)), ((), ())), preferred_element_type=jnp.float32
+        )
+
+
+def first_product(start, slab, chunks):
+    rows, width = start.shape
+    cols = slab.shape[1]
+    return pl.pallas_call(
+        sketch_kernel,
+        out_shape=[jax.ShapeDtypeStruct((width, cols // chunks), jnp.float32)] * chunks,
+        in_specs=[pl.BlockSpec(memory_space=pl.ANY)] * 2,
+        out_specs=[pl.BlockSpec(memory_space=pltpu.VMEM)] * chunks,
+        scratch_shapes=[
+            pltpu.VMEM((rows, width), jnp.bfloat16),
+            pltpu.VMEM((cols // TILE, rows, TILE), jnp.bfloat16),
+            pltpu.SemaphoreType.DMA,
+            pltpu.SemaphoreType.DMA((cols // TILE,)),
+        ],
+        compiler_params=pltpu.CompilerParams(vmem_limit_bytes=KERNEL_VMEM),
+        cost_estimate=pl.CostEstimate(
+            flops=2 * rows * width * cols, bytes_accessed=2 * rows * cols, transcendentals=0
+        ),
+        name="first_product",
+    )(start, slab)
 
 
 def matmul(left, right, exact=True):
@@ -112,13 +163,13 @@
 UPDATES = 4
 LOOSE_UPDATES = 2
 CLOSE = 1e-5
-TILE = 1024
 
 
 def basis_kernel(
     total_cols, root_rows, gram_ref, mine_ref, other_ref, slab_ref,
-    basis_ref, product_ref, work_ref, inverse_ref,
+    basis_ref, product_ref, work_ref, inverse_ref, buffer, arrived,
 ):
+    copies = fetch_tiles(slab_ref, buffer, arrived)
     width = gram_ref.shape[0]
     row = lax.broadcasted_iota(jnp.int32, (width, width), 0)
     col = lax.broadcasted_iota(jnp.int32, (width, width), 1)
@@ -170,12 +221,12 @@
     high = basis.astype(jnp.bfloat16)
     low = (basis - high.astype(jnp.float32)).astype(jnp.bfloat16)
     pair = jnp.concatenate([high, low], axis=1).T
-    for start in range(0, slab_ref.shape[1], TILE):
-        tile = slab_ref[:, start : start + TILE]
+    for tile, copy in enumerate(copies):
+        copy.wait()
         both = lax.dot_general(
-            pair, tile, (((1,), (0,)), ((), ())), preferred_element_type=jnp.float32
-        )
-        product_ref[:, start : start + TILE] = both[:width] + both[width:]
+            pair, buffer[tile], (((1,), (0,)), ((), ())), preferred_element_type=jnp.float32
+        )
+        product_ref[:, tile * TILE : (tile + 1) * TILE] = both[:width] + both[width:]
 
 
 def make_basis(gram, mine, other, slab, total_cols, root_rows):
@@ -186,13 +237,16 @@
             jax.ShapeDtypeStruct((rows, width), jnp.float32),
             jax.ShapeDtypeStruct((width, slab.shape[1]), jnp.float32),
         ),
-        in_specs=[pl.BlockSpec(memory_space=pltpu.VMEM)] * 4,
+        in_specs=[pl.BlockSpec(memory_space=pltpu.VMEM)] * 3
+        + [pl.BlockSpec(memory_space=pl.ANY)],
         out_specs=[pl.BlockSpec(memory_space=pltpu.VMEM)] * 2,
         scratch_shapes=[
             pltpu.VMEM((width, width), jnp.float32),
             pltpu.VMEM((width, width), jnp.float32),
+            pltpu.VMEM((slab.shape[1] // TILE, rows, TILE), jnp.bfloat16),
+            pltpu.SemaphoreType.DMA((slab.shape[1] // TILE,)),
         ],
-        compiler_params=pltpu.CompilerParams(vmem_limit_bytes=24 * 2**20),
+        compiler_params=pltpu.CompilerParams(vmem_limit_bytes=KERNEL_VMEM),
         name="make_basis",
     )(gram, mine, other, slab)
 
@@ -208,20 +262,17 @@
     cols_chunk = cols_here // CHUNKS
     spans = [slice(c * cols_chunk, (c + 1) * cols_chunk) for c in range(CHUNKS)]
 
+    local_cols = first_product(start_sketch, activations, SKETCH_CHUNKS)
     partial_sketch = 0.0
     orders = orders_of("row")
     step = cols_here // SKETCH_CHUNKS
     for c in range(SKETCH_CHUNKS):
-        span, order = slice(c * step, (c + 1) * step), orders[c % 2]
-        local_cols = lax.dot_general(
+        span = slice(c * step, (c + 1) * step)
+        shared = sum_and_share(local_cols[c], "row", orders[c % 2], 1.0 / root_rows)
+        partial_sketch = partial_sketch + lax.dot_general(
             activations[:, span],
-            start_sketch,
-            (((0,), (0,)), ((), ())),
-            preferred_element_type=jnp.float32,
-        )
-        partial_sketch = partial_sketch + jnp.dot(
-            activations[:, span],
-            sum_and_share(local_cols, "row", order, 1.0 / root_rows),
+            shared,
+            (((1,), (1,)), ((), ())),
             preferred_element_type=jnp.float32,
         )
     other_sketch = swap(partial_sketch, "col", 1)

time: 89.7 us -> 87.2 us (0.972)
  matrix products: 9.12 us -> 2.35 us
  Pallas kernels: 4.43 us -> 9.28 us
  starting transfers between devices: 38.9 us -> 41.6 us
  local copies, waits for them, and re-layouts: 3.34 us -> 1.17 us
  waiting for transfers between devices: 30.8 us -> 29.9 us
    dot_general x8 -> x4, matrix products: 8.51 us -> 1.74 us  [per_device(): lax.dot_general(activations[:, span], shared, (((1,), (1,)), ((), ())), p...]
    pallas_call x0 -> x1, Pallas kernels: none -> 3.13 us  [first_product(): pl.pallas_call(sketch_kernel, out_shape=[jax.ShapeDtypeStruct((width, col...]
    ppermute x32, starting transfers between devices: 38.9 us -> 41.6 us  [swap(): return lax.ppermute(value, axis, [(i, i ^ distance) for i in range(size)])]
    unnamed x6 -> x4, local copies, waits for them, and re-layouts: 3.07 us -> 0.9 us
    pallas_call x1, Pallas kernels: 4.43 us -> 6.15 us  [make_basis(): pl.pallas_call(functools.partial(basis_kernel, total_cols, root_rows), ou...]
  transfers between devices with their start and end apart: 32 -> 32, of which waited for: 19 -> 18; matrix products, arithmetic and copies ran while one was open for 8% -> 3% of each run, Pallas kernels for 0% -> 0%
where the time goes in v9:
time: 87.2 us; the launch traced here: 87.1 us
  starting transfers between devices  41.6 us (48%)
  waiting for transfers between devices  29.9 us (34%)
  Pallas kernels  9.28 us (11%)
  matrix products  2.35 us (3%)
  other arithmetic  1.81 us (2%)
  local copies, waits for them, and re-layouts  1.17 us (1%)
  between operations  0.98 us (1%)
    ppermute x32, starting transfers between devices, swap(): return lax.ppermute(value, axis, [(i, i ^ distance) for i in range(size)])  41.6 us
    ppermute x32, waiting for transfers between devices, swap(): return lax.ppermute(value, axis, [(i, i ^ distance) for i in range(size)])  29.9 us
    pallas_call x1, Pallas kernels, make_basis(): pl.pallas_call(functools.partial(basis_kernel, total_cols, root_rows), ou...  6.15 us
    pallas_call x1, Pallas kernels, first_product(): pl.pallas_call(sketch_kernel, out_shape=[jax.ShapeDtypeStruct((width, col...  3.13 us
  transfers between devices with their start and end apart: 32, of which 18 were waited for; matrix products, arithmetic and copies ran while one was open for 3% of the time, Pallas kernels for 0%

profile of v9, /device:TPU:0, one launch (start us, length us, event | category | flops | bytes accessed | tf_op | source)
XLA Modules:
  0.0 87.1 jit_solution(17667820238609946567)
XLA Ops:
  0.7 0.9 %copy-done = bf16[512,128]{1,0:T(8,128)(2,1)S(1)} copy-done((bf16[512,128]{1,0:T(8,128)(2,1)S(1)}, bf16[512,128]{1,0:T(8,128)(2,1)}, u32[]{:S(2)}) %copy-start) | copy-done | bytes 131096
  1.6 3.1 %first_product.1 = (f32[128,1024]{1,0:T(8,128)S(1)}, f32[128,1024]{1,0:T(8,128)S(1)}, f32[128,1024]{1,0:T(8,128)S(1)}, f32[128,1024]{1,0:T(8,128)S(1)}) custom-call(bf16[512,128]{1,0:T(8,128)(2,1)S(1)} %copy-done, bf16[512,4096]{1,0:T(8,128)(2,1)} %slab_ref.3), custom_call_target="tpu_custom_call" | custom-call | flops 536870912 | bytes 4194304 | tf_op jit(solution)/shard_map/first_product/pallas_call | solution.py:120
  4.7 3.1 %collective-permute-start.15 = (bf16[128,512]{1,0:T(8,128)(2,1)S(1)}, bf16[128,512]{1,0:T(8,128)(2,1)S(1)}, u32[]{:S(2)}, u32[]{:S(2)}) collective-permute-start(bf16[128,512]{1,0:T(8,128)(2,1)S(1)} %select_convert_fusion), channel_id=1, source_target_pairs={{0,4},{2,6},{4,0},{6,2},{8,12},{10,14},{12,8},{14,10},{1,5},{3,7},... | collective-permute-start | bytes 393224 | tf_op jit(solution)/shard_map/ppermute | solution.py:28
  7.8 1.6 %collective-permute-start.10 = (bf16[128,512]{1,0:T(8,128)(2,1)S(1)}, bf16[128,512]{1,0:T(8,128)(2,1)S(1)}, u32[]{:S(2)}, u32[]{:S(2)}) collective-permute-start(bf16[128,512]{1,0:T(8,128)(2,1)S(1)} %select_convert_fusion.1), channel_id=1, source_target_pairs={{0,2},{2,0},{4,6},{6,4},{8,10},{10,8},{12,14},{14,12},{1,3},{3,1},... | collective-permute-start | bytes 393224 | tf_op jit(solution)/shard_map/ppermute | solution.py:28
  9.4 0.5 collective-permute-start.5
  10.2 1.6 %collective-permute-done.15 = bf16[128,512]{1,0:T(8,128)(2,1)S(1)} collective-permute-done((bf16[128,512]{1,0:T(8,128)(2,1)S(1)}, bf16[128,512]{1,0:T(8,128)(2,1)S(1)}, u32[]{:S(2)}, u32[]{:S(2)}) %collective-permute-start.15) | collective-permute-done | bytes 131104 | tf_op jit(solution)/shard_map/ppermute | solution.py:28
  11.8 2.4 %collective-permute-start.16 = (bf16[128,256]{1,0:T(8,128)(2,1)S(1)}, bf16[128,256]{1,0:T(8,128)(2,1)S(1)}, u32[]{:S(2)}, u32[]{:S(2)}) collective-permute-start(bf16[128,256]{1,0:T(8,128)(2,1)S(1)} %select_convert_fusion.4), channel_id=1, source_target_pairs={{0,2},{2,0},{4,6},{6,4},{8,10},{10,8},{12,14},{14,12},{1,3},{3,1},... | collective-permute-start | bytes 196616 | tf_op jit(solution)/shard_map/ppermute | solution.py:28
  14.3 1.7 %collective-permute-start.11 = (bf16[128,256]{1,0:T(8,128)(2,1)S(1)}, bf16[128,256]{1,0:T(8,128)(2,1)S(1)}, u32[]{:S(2)}, u32[]{:S(2)}) collective-permute-start(bf16[128,256]{1,0:T(8,128)(2,1)S(1)} %select_convert_fusion.5), channel_id=1, source_target_pairs={{0,4},{2,6},{4,0},{6,2},{8,12},{10,14},{12,8},{14,10},{1,5},{3,7},... | collective-permute-start | bytes 196616 | tf_op jit(solution)/shard_map/ppermute | solution.py:28
  16.1 0.6 collective-permute-start.6
  16.8 1.5 %collective-permute-start.1 = (bf16[128,256]{1,0:T(8,128)(2,1)S(1)}, bf16[128,256]{1,0:T(8,128)(2,1)S(1)}, u32[]{:S(2)}, u32[]{:S(2)}) collective-permute-start(bf16[128,256]{1,0:T(8,128)(2,1)S(1)} %select_convert_fusion.7), channel_id=1, source_target_pairs={{0,4},{2,6},{4,0},{6,2},{8,12},{10,14},{12,8},{14,10},{1,5},{3,7},... | collective-permute-start | bytes 196616 | tf_op jit(solution)/shard_map/ppermute | solution.py:28
  18.3 2.7 %collective-permute-start.17 = (bf16[128,256]{1,0:T(8,128)(2,1)S(1)}, bf16[128,256]{1,0:T(8,128)(2,1)S(1)}, u32[]{:S(2)}, u32[]{:S(2)}) collective-permute-start(bf16[128,256]{1,0:T(8,128)(2,1)S(1)} %fusion.31), channel_id=1, source_target_pairs={{0,8},{2,10},{4,12},{6,14},{8,0},{10,2},{12,4},{14,6},{1,9},{3,11}... | collective-permute-start | bytes 196616 | tf_op jit(solution)/shard_map/ppermute | solution.py:28
  21.0 0.9 %collective-permute-start.12 = (bf16[128,256]{1,0:T(8,128)(2,1)S(1)}, bf16[128,256]{1,0:T(8,128)(2,1)S(1)}, u32[]{:S(2)}, u32[]{:S(2)}) collective-permute-start(bf16[128,256]{1,0:T(8,128)(2,1)S(1)} %fusion.30), channel_id=1, source_target_pairs={{0,8},{2,10},{4,12},{6,14},{8,0},{10,2},{12,4},{14,6},{1,9},{3,11}... | collective-permute-start | bytes 196616 | tf_op jit(solution)/shard_map/ppermute | solution.py:28
  21.9 2.2 %collective-permute-start.7 = (bf16[128,256]{1,0:T(8,128)(2,1)S(1)}, bf16[128,256]{1,0:T(8,128)(2,1)S(1)}, u32[]{:S(2)}, u32[]{:S(2)}) collective-permute-start(bf16[128,256]{1,0:T(8,128)(2,1)S(1)} %fusion.29), channel_id=1, source_target_pairs={{0,8},{2,10},{4,12},{6,14},{8,0},{10,2},{12,4},{14,6},{1,9},{3,11}... | collective-permute-start | bytes 196616 | tf_op jit(solution)/shard_map/ppermute | solution.py:28
  24.1 0.9 %collective-permute-start.2 = (bf16[128,256]{1,0:T(8,128)(2,1)S(1)}, bf16[128,256]{1,0:T(8,128)(2,1)S(1)}, u32[]{:S(2)}, u32[]{:S(2)}) collective-permute-start(bf16[128,256]{1,0:T(8,128)(2,1)S(1)} %fusion.28), channel_id=1, source_target_pairs={{0,8},{2,10},{4,12},{6,14},{8,0},{10,2},{12,4},{14,6},{1,9},{3,11}... | collective-permute-start | bytes 196616 | tf_op jit(solution)/shard_map/ppermute | solution.py:28
  25.0 2.2 %collective-permute-done.17 = bf16[128,256]{1,0:T(8,128)(2,1)S(1)} collective-permute-done((bf16[128,256]{1,0:T(8,128)(2,1)S(1)}, bf16[128,256]{1,0:T(8,128)(2,1)S(1)}, u32[]{:S(2)}, u32[]{:S(2)}) %collective-permute-start.17) | collective-permute-done | bytes 65568 | tf_op jit(solution)/shard_map/ppermute | solution.py:28
  27.2 1.8 %collective-permute-start.18 = (bf16[128,256]{1,0:T(8,128)(2,1)S(1)}, bf16[128,256]{1,0:T(8,128)(2,1)S(1)}, u32[]{:S(2)}, u32[]{:S(2)}) collective-permute-start(bf16[128,256]{1,0:T(8,128)(2,1)S(1)} %multiply_convert_fusion), channel_id=1, source_target_pairs={{0,2},{2,0},{4,6},{6,4},{8,10},{10,8},{12,14},{14,12},{1,3},{3,1},... | collective-permute-start | bytes 196616 | tf_op jit(solution)/shard_map/ppermute | solution.py:28
  29.0 1.1 %collective-permute-done.12 = bf16[128,256]{1,0:T(8,128)(2,1)S(1)} collective-permute-done((bf16[128,256]{1,0:T(8,128)(2,1)S(1)}, bf16[128,256]{1,0:T(8,128)(2,1)S(1)}, u32[]{:S(2)}, u32[]{:S(2)}) %collective-permute-start.12) | collective-permute-done | bytes 65568 | tf_op jit(solution)/shard_map/ppermute | solution.py:28
  30.2 1.0 %collective-permute-done.7 = bf16[128,256]{1,0:T(8,128)(2,1)S(1)} collective-permute-done((bf16[128,256]{1,0:T(8,128)(2,1)S(1)}, bf16[128,256]{1,0:T(8,128)(2,1)S(1)}, u32[]{:S(2)}, u32[]{:S(2)}) %collective-permute-start.7) | collective-permute-done | bytes 65568 | tf_op jit(solution)/shard_map/ppermute | solution.py:28
  31.3 1.2 %collective-permute-start.8 = (bf16[128,256]{1,0:T(8,128)(2,1)S(1)}, bf16[128,256]{1,0:T(8,128)(2,1)S(1)}, u32[]{:S(2)}, u32[]{:S(2)}) collective-permute-start(bf16[128,256]{1,0:T(8,128)(2,1)S(1)} %multiply_convert_fusion.2), channel_id=1, source_target_pairs={{0,2},{2,0},{4,6},{6,4},{8,10},{10,8},{12,14},{14,12},{1,3},{3,1},... | collective-permute-start | bytes 196616 | tf_op jit(solution)/shard_map/ppermute | solution.py:28
  32.5 1.1 %collective-permute-start.3 = (bf16[128,256]{1,0:T(8,128)(2,1)S(1)}, bf16[128,256]{1,0:T(8,128)(2,1)S(1)}, u32[]{:S(2)}, u32[]{:S(2)}) collective-permute-start(bf16[128,256]{1,0:T(8,128)(2,1)S(1)} %multiply_convert_fusion.3), channel_id=1, source_target_pairs={{0,4},{2,6},{4,0},{6,2},{8,12},{10,14},{12,8},{14,10},{1,5},{3,7},... | collective-permute-start | bytes 196616 | tf_op jit(solution)/shard_map/ppermute | solution.py:28
  33.6 1.0 %collective-permute-start.19 = (bf16[128,512]{1,0:T(8,128)(2,1)S(1)}, bf16[128,512]{1,0:T(8,128)(2,1)S(1)}, u32[]{:S(2)}, u32[]{:S(2)}) collective-permute-start(bf16[128,512]{1,0:T(8,128)(2,1)S(1)} %pad_maximum_fusion.4), channel_id=1, source_target_pairs={{0,4},{2,6},{4,0},{6,2},{8,12},{10,14},{12,8},{14,10},{1,5},{3,7},... | collective-permute-start | bytes 393224 | tf_op jit(solution)/shard_map/ppermute | solution.py:28
  34.7 0.5 collective-permute-done.13
  35.2 1.2 %collective-permute-start.14 = (bf16[128,512]{1,0:T(8,128)(2,1)S(1)}, bf16[128,512]{1,0:T(8,128)(2,1)S(1)}, u32[]{:S(2)}, u32[]{:S(2)}) collective-permute-start(bf16[128,512]{1,0:T(8,128)(2,1)S(1)} %pad_maximum_fusion.3), channel_id=1, source_target_pairs={{0,2},{2,0},{4,6},{6,4},{8,10},{10,8},{12,14},{14,12},{1,3},{3,1},... | collective-permute-start | bytes 393224 | tf_op jit(solution)/shard_map/ppermute | solution.py:28
  36.5 0.9 %collective-permute-start.9 = (bf16[128,512]{1,0:T(8,128)(2,1)S(1)}, bf16[128,512]{1,0:T(8,128)(2,1)S(1)}, u32[]{:S(2)}, u32[]{:S(2)}) collective-permute-start(bf16[128,512]{1,0:T(8,128)(2,1)S(1)} %pad_maximum_fusion.2), channel_id=1, source_target_pairs={{0,4},{2,6},{4,0},{6,2},{8,12},{10,14},{12,8},{14,10},{1,5},{3,7},... | collective-permute-start | bytes 393224 | tf_op jit(solution)/shard_map/ppermute | solution.py:28
  37.6 1.1 %collective-permute-start.4 = (bf16[128,512]{1,0:T(8,128)(2,1)S(1)}, bf16[128,512]{1,0:T(8,128)(2,1)S(1)}, u32[]{:S(2)}, u32[]{:S(2)}) collective-permute-start(bf16[128,512]{1,0:T(8,128)(2,1)S(1)} %pad_maximum_fusion.1), channel_id=1, source_target_pairs={{0,2},{2,0},{4,6},{6,4},{8,10},{10,8},{12,14},{14,12},{1,3},{3,1},... | collective-permute-start | bytes 393224 | tf_op jit(solution)/shard_map/ppermute | solution.py:28
  38.7 1.4 %collective-permute-done.19 = bf16[128,512]{1,0:T(8,128)(2,1)S(1)} collective-permute-done((bf16[128,512]{1,0:T(8,128)(2,1)S(1)}, bf16[128,512]{1,0:T(8,128)(2,1)S(1)}, u32[]{:S(2)}, u32[]{:S(2)}) %collective-permute-start.19) | collective-permute-done | bytes 131104 | tf_op jit(solution)/shard_map/ppermute | solution.py:28
  42.0 0.6 collective-permute-done.4
  42.7 0.4 fusion.2.mine_ref
  43.2 1.5 %collective-permute-done.20.other_ref = f32[512,128]{1,0:T(8,128)S(1)} collective-permute-done((f32[512,128]{1,0:T(8,128)S(1)}, f32[512,128]{1,0:T(8,128)S(1)}, u32[]{:S(2)}, u32[]{:S(2)}) %collective-permute-start.20) | collective-permute-done | bytes 262176 | tf_op jit(solution)/shard_map/ppermute | solution.py:28
  44.7 0.6 fusion.24
  45.3 1.1 %collective-permute-start.21 = (f32[128,128]{1,0:T(8,128)S(1)}, f32[128,128]{1,0:T(8,128)S(1)}, u32[]{:S(2)}, u32[]{:S(2)}) collective-permute-start(f32[128,128]{1,0:T(8,128)S(1)} %fusion.24), channel_id=1, source_target_pairs={{0,2},{2,0},{4,6},{6,4},{8,10},{10,8},{12,14},{14,12},{1,3},{3,1},... | collective-permute-start | bytes 196616 | tf_op jit(solution)/shard_map/ppermute | solution.py:28
  46.4 3.3 %collective-permute-done.21 = f32[128,128]{1,0:T(8,128)S(1)} collective-permute-done((f32[128,128]{1,0:T(8,128)S(1)}, f32[128,128]{1,0:T(8,128)S(1)}, u32[]{:S(2)}, u32[]{:S(2)}) %collective-permute-start.21) | collective-permute-done | bytes 65568 | tf_op jit(solution)/shard_map/ppermute | solution.py:28
  49.7 1.1 %collective-permute-start.22 = (f32[128,128]{1,0:T(8,128)S(1)}, f32[128,128]{1,0:T(8,128)S(1)}, u32[]{:S(2)}, u32[]{:S(2)}) collective-permute-start(f32[128,128]{1,0:T(8,128)S(1)} %add.128), channel_id=1, source_target_pairs={{0,4},{2,6},{4,0},{6,2},{8,12},{10,14},{12,8},{14,10},{1,5},{3,7},... | collective-permute-start | bytes 196616 | tf_op jit(solution)/shard_map/ppermute | solution.py:28
  50.8 3.2 %collective-permute-done.22 = f32[128,128]{1,0:T(8,128)S(1)} collective-permute-done((f32[128,128]{1,0:T(8,128)S(1)}, f32[128,128]{1,0:T(8,128)S(1)}, u32[]{:S(2)}, u32[]{:S(2)}) %collective-permute-start.22) | collective-permute-done | bytes 65568 | tf_op jit(solution)/shard_map/ppermute | solution.py:28
  54.0 1.9 %collective-permute-start.23 = (f32[128,128]{1,0:T(8,128)S(1)}, f32[128,128]{1,0:T(8,128)S(1)}, u32[]{:S(2)}, u32[]{:S(2)}) collective-permute-start(f32[128,128]{1,0:T(8,128)S(1)} %add.129), channel_id=1, source_target_pairs={{0,8},{2,10},{4,12},{6,14},{8,0},{10,2},{12,4},{14,6},{1,9},{3,11}... | collective-permute-start | bytes 196616 | tf_op jit(solution)/shard_map/ppermute | solution.py:28
  55.9 4.0 %collective-permute-done.23 = f32[128,128]{1,0:T(8,128)S(1)} collective-permute-done((f32[128,128]{1,0:T(8,128)S(1)}, f32[128,128]{1,0:T(8,128)S(1)}, u32[]{:S(2)}, u32[]{:S(2)}) %collective-permute-start.23) | collective-permute-done | bytes 65568 | tf_op jit(solution)/shard_map/ppermute | solution.py:28
  60.0 6.1 %make_basis.1 = (f32[512,128]{1,0:T(8,128)}, f32[128,4096]{1,0:T(8,128)S(1)}) custom-call(f32[128,128]{1,0:T(8,128)S(1)} %add.130.gram_ref, f32[512,128]{1,0:T(8,128)S(1)} %fusion.2.mine_ref, f32[512,128]{1,0:T(8,128)S(1)} %collective-permute-done.20.other_ref, bf16[512,4096]{1,0:T(8,128)(2,1)} %slab_ref.3), custom_call_target="tpu_custom_call" | custom-call | tf_op jit(solution)/shard_map/make_basis/pallas_call | solution.py:234
  66.3 1.1 %collective-permute-start.28 = (bf16[4,16,2048]{2,1,0:T(8,128)(2,1)S(1)}, bf16[4,16,2048]{2,1,0:T(8,128)(2,1)S(1)}, u32[]{:S(2)}, u32[]{:S(2)}) collective-permute-start(bf16[4,16,2048]{2,1,0:T(8,128)(2,1)S(1)} %fusion.11), channel_id=1, source_target_pairs={{0,2},{2,0},{4,6},{6,4},{8,10},{10,8},{12,14},{14,12},{1,3},{3,1},... | collective-permute-start | bytes 786440 | tf_op jit(solution)/shard_map/ppermute | solution.py:28
  67.4 1.1 %collective-permute-start.24 = (bf16[4,16,2048]{2,1,0:T(8,128)(2,1)S(1)}, bf16[4,16,2048]{2,1,0:T(8,128)(2,1)S(1)}, u32[]{:S(2)}, u32[]{:S(2)}) collective-permute-start(bf16[4,16,2048]{2,1,0:T(8,128)(2,1)S(1)} %fusion.10), channel_id=1, source_target_pairs={{0,2},{2,0},{4,6},{6,4},{8,10},{10,8},{12,14},{14,12},{1,3},{3,1},... | collective-permute-start | bytes 786440 | tf_op jit(solution)/shard_map/ppermute | solution.py:28
  68.5 5.6 %collective-permute-done.28 = bf16[4,16,2048]{2,1,0:T(8,128)(2,1)S(1)} collective-permute-done((bf16[4,16,2048]{2,1,0:T(8,128)(2,1)S(1)}, bf16[4,16,2048]{2,1,0:T(8,128)(2,1)S(1)}, u32[]{:S(2)}, u32[]{:S(2)}) %collective-permute-start.28) | collective-permute-done | bytes 262176 | tf_op jit(solution)/shard_map/ppermute | solution.py:28
  74.2 1.2 %collective-permute-start.31 = (bf16[1,16,2048]{2,1,0:T(8,128)(2,1)S(1)}, bf16[1,16,2048]{2,1,0:T(8,128)(2,1)S(1)}, u32[]{:S(2)}, u32[]{:S(2)}) collective-permute-start(bf16[1,16,2048]{2,1,0:T(8,128)(2,1)S(1)} %get-tuple-element.20), channel_id=1, source_target_pairs={{0,12},{2,14},{4,8},{6,10},{8,4},{10,6},{12,0},{14,2},{1,13},{3,15... | collective-permute-start | bytes 196616 | tf_op jit(solution)/shard_map/ppermute | solution.py:28
  75.4 0.7 collective-permute-start.30
  76.2 2.5 %collective-permute-start.29 = (bf16[1,16,2048]{2,1,0:T(8,128)(2,1)S(1)}, bf16[1,16,2048]{2,1,0:T(8,128)(2,1)S(1)}, u32[]{:S(2)}, u32[]{:S(2)}) collective-permute-start(bf16[1,16,2048]{2,1,0:T(8,128)(2,1)S(1)} %get-tuple-element.19), channel_id=1, source_target_pairs={{0,4},{2,6},{4,0},{6,2},{8,12},{10,14},{12,8},{14,10},{1,5},{3,7},... | collective-permute-start | bytes 196616 | tf_op jit(solution)/shard_map/ppermute | solution.py:28
  78.8 1.2 %collective-permute-start.27 = (bf16[1,16,2048]{2,1,0:T(8,128)(2,1)S(1)}, bf16[1,16,2048]{2,1,0:T(8,128)(2,1)S(1)}, u32[]{:S(2)}, u32[]{:S(2)}) collective-permute-start(bf16[1,16,2048]{2,1,0:T(8,128)(2,1)S(1)} %get-tuple-element.17), channel_id=1, source_target_pairs={{0,12},{2,14},{4,8},{6,10},{8,4},{10,6},{12,0},{14,2},{1,13},{3,15... | collective-permute-start | bytes 196616 | tf_op jit(solution)/shard_map/ppermute | solution.py:28
  80.4 2.8 %collective-permute-start.25 = (bf16[1,16,2048]{2,1,0:T(8,128)(2,1)S(1)}, bf16[1,16,2048]{2,1,0:T(8,128)(2,1)S(1)}, u32[]{:S(2)}, u32[]{:S(2)}) collective-permute-start(bf16[1,16,2048]{2,1,0:T(8,128)(2,1)S(1)} %get-tuple-element.16), channel_id=1, source_target_pairs={{0,4},{2,6},{4,0},{6,2},{8,12},{10,14},{12,8},{14,10},{1,5},{3,7},... | collective-permute-start | bytes 196616 | tf_op jit(solution)/shard_map/ppermute | solution.py:28
  83.3 1.7 %collective-permute-done.27 = bf16[1,16,2048]{2,1,0:T(8,128)(2,1)S(1)} collective-permute-done((bf16[1,16,2048]{2,1,0:T(8,128)(2,1)S(1)}, bf16[1,16,2048]{2,1,0:T(8,128)(2,1)S(1)}, u32[]{:S(2)}, u32[]{:S(2)}) %collective-permute-start.27) | collective-permute-done | bytes 65568 | tf_op jit(solution)/shard_map/ppermute | solution.py:28
  84.9 1.3 %collective-permute-done.26 = bf16[1,16,2048]{2,1,0:T(8,128)(2,1)S(1)} collective-permute-done((bf16[1,16,2048]{2,1,0:T(8,128)(2,1)S(1)}, bf16[1,16,2048]{2,1,0:T(8,128)(2,1)S(1)}, u32[]{:S(2)}, u32[]{:S(2)}) %collective-permute-start.26) | collective-permute-done | bytes 65568 | tf_op jit(solution)/shard_map/ppermute | solution.py:28
  86.3 0.7 pad_maximum_fusion
  (72 shorter events, 4.1 us)
Async XLA Ops:
  0.6 0.9 %copy-start = (bf16[512,128]{1,0:T(8,128)(2,1)S(1)}, bf16[512,128]{1,0:T(8,128)(2,1)}, u32[]{:S(2)}) copy-start(bf16[512,128]{1,0:T(8,128)(2,1)} %start_ref.1) | copy-start | bytes 393220
  4.7 7.0 %collective-permute-start.15 = (bf16[128,512]{1,0:T(8,128)(2,1)S(1)}, bf16[128,512]{1,0:T(8,128)(2,1)S(1)}, u32[]{:S(2)}, u32[]{:S(2)}) collective-permute-start(bf16[128,512]{1,0:T(8,128)(2,1)S(1)} %select_convert_fusion), channel_id=1, source_target_pairs={{0,4},{2,6},{4,0},{6,2},{8,12},{10,14},{12,8},{14,10},{1,5},{3,7},... | collective-permute-start | bytes 393224 | tf_op jit(solution)/shard_map/ppermute | solution.py:28
  7.8 6.3 %collective-permute-start.10 = (bf16[128,512]{1,0:T(8,128)(2,1)S(1)}, bf16[128,512]{1,0:T(8,128)(2,1)S(1)}, u32[]{:S(2)}, u32[]{:S(2)}) collective-permute-start(bf16[128,512]{1,0:T(8,128)(2,1)S(1)} %select_convert_fusion.1), channel_id=1, source_target_pairs={{0,2},{2,0},{4,6},{6,4},{8,10},{10,8},{12,14},{14,12},{1,3},{3,1},... | collective-permute-start | bytes 393224 | tf_op jit(solution)/shard_map/ppermute | solution.py:28
  9.4 6.6 %collective-permute-start.5 = (bf16[128,512]{1,0:T(8,128)(2,1)S(1)}, bf16[128,512]{1,0:T(8,128)(2,1)S(1)}, u32[]{:S(2)}, u32[]{:S(2)}) collective-permute-start(bf16[128,512]{1,0:T(8,128)(2,1)S(1)} %select_convert_fusion.2), channel_id=1, source_target_pairs={{0,4},{2,6},{4,0},{6,2},{8,12},{10,14},{12,8},{14,10},{1,5},{3,7},... | collective-permute-start | bytes 393224 | tf_op jit(solution)/shard_map/ppermute | solution.py:28
  10.0 6.7 %collective-permute-start = (bf16[128,512]{1,0:T(8,128)(2,1)S(1)}, bf16[128,512]{1,0:T(8,128)(2,1)S(1)}, u32[]{:S(2)}, u32[]{:S(2)}) collective-permute-start(bf16[128,512]{1,0:T(8,128)(2,1)S(1)} %select_convert_fusion.3), channel_id=1, source_target_pairs={{0,2},{2,0},{4,6},{6,4},{8,10},{10,8},{12,14},{14,12},{1,3},{3,1},... | collective-permute-start | bytes 393224 | tf_op jit(solution)/shard_map/ppermute | solution.py:28
  11.8 6.5 %collective-permute-start.16 = (bf16[128,256]{1,0:T(8,128)(2,1)S(1)}, bf16[128,256]{1,0:T(8,128)(2,1)S(1)}, u32[]{:S(2)}, u32[]{:S(2)}) collective-permute-start(bf16[128,256]{1,0:T(8,128)(2,1)S(1)} %select_convert_fusion.4), channel_id=1, source_target_pairs={{0,2},{2,0},{4,6},{6,4},{8,10},{10,8},{12,14},{14,12},{1,3},{3,1},... | collective-permute-start | bytes 196616 | tf_op jit(solution)/shard_map/ppermute | solution.py:28
  14.2 25.9 %copy-start.1 = (bf16[512,4096]{1,0:T(8,128)(2,1)S(1)}, bf16[512,4096]{1,0:T(8,128)(2,1)}, u32[]{:S(2)}) copy-start(bf16[512,4096]{1,0:T(8,128)(2,1)} %slab_ref.3) | copy-start | bytes 12582916
  14.3 6.7 %collective-permute-start.11 = (bf16[128,256]{1,0:T(8,128)(2,1)S(1)}, bf16[128,256]{1,0:T(8,128)(2,1)S(1)}, u32[]{:S(2)}, u32[]{:S(2)}) collective-permute-start(bf16[128,256]{1,0:T(8,128)(2,1)S(1)} %select_convert_fusion.5), channel_id=1, source_target_pairs={{0,4},{2,6},{4,0},{6,2},{8,12},{10,14},{12,8},{14,10},{1,5},{3,7},... | collective-permute-start | bytes 196616 | tf_op jit(solution)/shard_map/ppermute | solution.py:28
  16.1 5.8 %collective-permute-start.6 = (bf16[128,256]{1,0:T(8,128)(2,1)S(1)}, bf16[128,256]{1,0:T(8,128)(2,1)S(1)}, u32[]{:S(2)}, u32[]{:S(2)}) collective-permute-start(bf16[128,256]{1,0:T(8,128)(2,1)S(1)} %select_convert_fusion.6), channel_id=1, source_target_pairs={{0,2},{2,0},{4,6},{6,4},{8,10},{10,8},{12,14},{14,12},{1,3},{3,1},... | collective-permute-start | bytes 196616 | tf_op jit(solution)/shard_map/ppermute | solution.py:28
  16.8 7.3 %collective-permute-start.1 = (bf16[128,256]{1,0:T(8,128)(2,1)S(1)}, bf16[128,256]{1,0:T(8,128)(2,1)S(1)}, u32[]{:S(2)}, u32[]{:S(2)}) collective-permute-start(bf16[128,256]{1,0:T(8,128)(2,1)S(1)} %select_convert_fusion.7), channel_id=1, source_target_pairs={{0,4},{2,6},{4,0},{6,2},{8,12},{10,14},{12,8},{14,10},{1,5},{3,7},... | collective-permute-start | bytes 196616 | tf_op jit(solution)/shard_map/ppermute | solution.py:28
  18.3 8.8 %collective-permute-start.17 = (bf16[128,256]{1,0:T(8,128)(2,1)S(1)}, bf16[128,256]{1,0:T(8,128)(2,1)S(1)}, u32[]{:S(2)}, u32[]{:S(2)}) collective-permute-start(bf16[128,256]{1,0:T(8,128)(2,1)S(1)} %fusion.31), channel_id=1, source_target_pairs={{0,8},{2,10},{4,12},{6,14},{8,0},{10,2},{12,4},{14,6},{1,9},{3,11}... | collective-permute-start | bytes 196616 | tf_op jit(solution)/shard_map/ppermute | solution.py:28
  21.0 9.1 %collective-permute-start.12 = (bf16[128,256]{1,0:T(8,128)(2,1)S(1)}, bf16[128,256]{1,0:T(8,128)(2,1)S(1)}, u32[]{:S(2)}, u32[]{:S(2)}) collective-permute-start(bf16[128,256]{1,0:T(8,128)(2,1)S(1)} %fusion.30), channel_id=1, source_target_pairs={{0,8},{2,10},{4,12},{6,14},{8,0},{10,2},{12,4},{14,6},{1,9},{3,11}... | collective-permute-start | bytes 196616 | tf_op jit(solution)/shard_map/ppermute | solution.py:28
  21.9 9.3 %collective-permute-start.7 = (bf16[128,256]{1,0:T(8,128)(2,1)S(1)}, bf16[128,256]{1,0:T(8,128)(2,1)S(1)}, u32[]{:S(2)}, u32[]{:S(2)}) collective-permute-start(bf16[128,256]{1,0:T(8,128)(2,1)S(1)} %fusion.29), channel_id=1, source_target_pairs={{0,8},{2,10},{4,12},{6,14},{8,0},{10,2},{12,4},{14,6},{1,9},{3,11}... | collective-permute-start | bytes 196616 | tf_op jit(solution)/shard_map/ppermute | solution.py:28
  24.1 8.3 %collective-permute-start.2 = (bf16[128,256]{1,0:T(8,128)(2,1)S(1)}, bf16[128,256]{1,0:T(8,128)(2,1)S(1)}, u32[]{:S(2)}, u32[]{:S(2)}) collective-permute-start(bf16[128,256]{1,0:T(8,128)(2,1)S(1)} %fusion.28), channel_id=1, source_target_pairs={{0,8},{2,10},{4,12},{6,14},{8,0},{10,2},{12,4},{14,6},{1,9},{3,11}... | collective-permute-start | bytes 196616 | tf_op jit(solution)/shard_map/ppermute | solution.py:28
  27.2 6.4 %collective-permute-start.18 = (bf16[128,256]{1,0:T(8,128)(2,1)S(1)}, bf16[128,256]{1,0:T(8,128)(2,1)S(1)}, u32[]{:S(2)}, u32[]{:S(2)}) collective-permute-start(bf16[128,256]{1,0:T(8,128)(2,1)S(1)} %multiply_convert_fusion), channel_id=1, source_target_pairs={{0,2},{2,0},{4,6},{6,4},{8,10},{10,8},{12,14},{14,12},{1,3},{3,1},... | collective-permute-start | bytes 196616 | tf_op jit(solution)/shard_map/ppermute | solution.py:28
  30.1 5.0 %collective-permute-start.13 = (bf16[128,256]{1,0:T(8,128)(2,1)S(1)}, bf16[128,256]{1,0:T(8,128)(2,1)S(1)}, u32[]{:S(2)}, u32[]{:S(2)}) collective-permute-start(bf16[128,256]{1,0:T(8,128)(2,1)S(1)} %multiply_convert_fusion.1), channel_id=1, source_target_pairs={{0,4},{2,6},{4,0},{6,2},{8,12},{10,14},{12,8},{14,10},{1,5},{3,7},... | collective-permute-start | bytes 196616 | tf_op jit(solution)/shard_map/ppermute | solution.py:28
  31.3 5.1 %collective-permute-start.8 = (bf16[128,256]{1,0:T(8,128)(2,1)S(1)}, bf16[128,256]{1,0:T(8,128)(2,1)S(1)}, u32[]{:S(2)}, u32[]{:S(2)}) collective-permute-start(bf16[128,256]{1,0:T(8,128)(2,1)S(1)} %multiply_convert_fusion.2), channel_id=1, source_target_pairs={{0,2},{2,0},{4,6},{6,4},{8,10},{10,8},{12,14},{14,12},{1,3},{3,1},... | collective-permute-start | bytes 196616 | tf_op jit(solution)/shard_map/ppermute | solution.py:28
  32.5 5.1 %collective-permute-start.3 = (bf16[128,256]{1,0:T(8,128)(2,1)S(1)}, bf16[128,256]{1,0:T(8,128)(2,1)S(1)}, u32[]{:S(2)}, u32[]{:S(2)}) collective-permute-start(bf16[128,256]{1,0:T(8,128)(2,1)S(1)} %multiply_convert_fusion.3), channel_id=1, source_target_pairs={{0,4},{2,6},{4,0},{6,2},{8,12},{10,14},{12,8},{14,10},{1,5},{3,7},... | collective-permute-start | bytes 196616 | tf_op jit(solution)/shard_map/ppermute | solution.py:28
  33.6 6.4 %collective-permute-start.19 = (bf16[128,512]{1,0:T(8,128)(2,1)S(1)}, bf16[128,512]{1,0:T(8,128)(2,1)S(1)}, u32[]{:S(2)}, u32[]{:S(2)}) collective-permute-start(bf16[128,512]{1,0:T(8,128)(2,1)S(1)} %pad_maximum_fusion.4), channel_id=1, source_target_pairs={{0,4},{2,6},{4,0},{6,2},{8,12},{10,14},{12,8},{14,10},{1,5},{3,7},... | collective-permute-start | bytes 393224 | tf_op jit(solution)/shard_map/ppermute | solution.py:28
  35.2 5.6 %collective-permute-start.14 = (bf16[128,512]{1,0:T(8,128)(2,1)S(1)}, bf16[128,512]{1,0:T(8,128)(2,1)S(1)}, u32[]{:S(2)}, u32[]{:S(2)}) collective-permute-start(bf16[128,512]{1,0:T(8,128)(2,1)S(1)} %pad_maximum_fusion.3), channel_id=1, source_target_pairs={{0,2},{2,0},{4,6},{6,4},{8,10},{10,8},{12,14},{14,12},{1,3},{3,1},... | collective-permute-start | bytes 393224 | tf_op jit(solution)/shard_map/ppermute | solution.py:28
  36.5 5.0 %collective-permute-start.9 = (bf16[128,512]{1,0:T(8,128)(2,1)S(1)}, bf16[128,512]{1,0:T(8,128)(2,1)S(1)}, u32[]{:S(2)}, u32[]{:S(2)}) collective-permute-start(bf16[128,512]{1,0:T(8,128)(2,1)S(1)} %pad_maximum_fusion.2), channel_id=1, source_target_pairs={{0,4},{2,6},{4,0},{6,2},{8,12},{10,14},{12,8},{14,10},{1,5},{3,7},... | collective-permute-start | bytes 393224 | tf_op jit(solution)/shard_map/ppermute | solution.py:28
  37.6 5.0 %collective-permute-start.4 = (bf16[128,512]{1,0:T(8,128)(2,1)S(1)}, bf16[128,512]{1,0:T(8,128)(2,1)S(1)}, u32[]{:S(2)}, u32[]{:S(2)}) collective-permute-start(bf16[128,512]{1,0:T(8,128)(2,1)S(1)} %pad_maximum_fusion.1), channel_id=1, source_target_pairs={{0,2},{2,0},{4,6},{6,4},{8,10},{10,8},{12,14},{14,12},{1,3},{3,1},... | collective-permute-start | bytes 393224 | tf_op jit(solution)/shard_map/ppermute | solution.py:28
  43.1 1.6 %collective-permute-start.20 = (f32[512,128]{1,0:T(8,128)S(1)}, f32[512,128]{1,0:T(8,128)S(1)}, u32[]{:S(2)}, u32[]{:S(2)}) collective-permute-start(f32[512,128]{1,0:T(8,128)S(1)} %fusion.2.mine_ref), channel_id=1, source_target_pairs={{0,1},{1,0},{2,3},{3,2},{4,5},{5,4},{6,7},{7,6},{8,9},{9,8},{10,11... | collective-permute-start | bytes 786440 | tf_op jit(solution)/shard_map/ppermute | solution.py:28
  45.3 4.3 %collective-permute-start.21 = (f32[128,128]{1,0:T(8,128)S(1)}, f32[128,128]{1,0:T(8,128)S(1)}, u32[]{:S(2)}, u32[]{:S(2)}) collective-permute-start(f32[128,128]{1,0:T(8,128)S(1)} %fusion.24), channel_id=1, source_target_pairs={{0,2},{2,0},{4,6},{6,4},{8,10},{10,8},{12,14},{14,12},{1,3},{3,1},... | collective-permute-start | bytes 196616 | tf_op jit(solution)/shard_map/ppermute | solution.py:28
  49.7 4.3 %collective-permute-start.22 = (f32[128,128]{1,0:T(8,128)S(1)}, f32[128,128]{1,0:T(8,128)S(1)}, u32[]{:S(2)}, u32[]{:S(2)}) collective-permute-start(f32[128,128]{1,0:T(8,128)S(1)} %add.128), channel_id=1, source_target_pairs={{0,4},{2,6},{4,0},{6,2},{8,12},{10,14},{12,8},{14,10},{1,5},{3,7},... | collective-permute-start | bytes 196616 | tf_op jit(solution)/shard_map/ppermute | solution.py:28
  54.0 5.9 %collective-permute-start.23 = (f32[128,128]{1,0:T(8,128)S(1)}, f32[128,128]{1,0:T(8,128)S(1)}, u32[]{:S(2)}, u32[]{:S(2)}) collective-permute-start(f32[128,128]{1,0:T(8,128)S(1)} %add.129), channel_id=1, source_target_pairs={{0,8},{2,10},{4,12},{6,14},{8,0},{10,2},{12,4},{14,6},{1,9},{3,11}... | collective-permute-start | bytes 196616 | tf_op jit(solution)/shard_map/ppermute | solution.py:28
  66.3 7.8 %collective-permute-start.28 = (bf16[4,16,2048]{2,1,0:T(8,128)(2,1)S(1)}, bf16[4,16,2048]{2,1,0:T(8,128)(2,1)S(1)}, u32[]{:S(2)}, u32[]{:S(2)}) collective-permute-start(bf16[4,16,2048]{2,1,0:T(8,128)(2,1)S(1)} %fusion.11), channel_id=1, source_target_pairs={{0,2},{2,0},{4,6},{6,4},{8,10},{10,8},{12,14},{14,12},{1,3},{3,1},... | collective-permute-start | bytes 786440 | tf_op jit(solution)/shard_map/ppermute | solution.py:28
  67.4 11.2 %collective-permute-start.24 = (bf16[4,16,2048]{2,1,0:T(8,128)(2,1)S(1)}, bf16[4,16,2048]{2,1,0:T(8,128)(2,1)S(1)}, u32[]{:S(2)}, u32[]{:S(2)}) collective-permute-start(bf16[4,16,2048]{2,1,0:T(8,128)(2,1)S(1)} %fusion.10), channel_id=1, source_target_pairs={{0,2},{2,0},{4,6},{6,4},{8,10},{10,8},{12,14},{14,12},{1,3},{3,1},... | collective-permute-start | bytes 786440 | tf_op jit(solution)/shard_map/ppermute | solution.py:28
  74.2 6.2 %collective-permute-start.31 = (bf16[1,16,2048]{2,1,0:T(8,128)(2,1)S(1)}, bf16[1,16,2048]{2,1,0:T(8,128)(2,1)S(1)}, u32[]{:S(2)}, u32[]{:S(2)}) collective-permute-start(bf16[1,16,2048]{2,1,0:T(8,128)(2,1)S(1)} %get-tuple-element.20), channel_id=1, source_target_pairs={{0,12},{2,14},{4,8},{6,10},{8,4},{10,6},{12,0},{14,2},{1,13},{3,15... | collective-permute-start | bytes 196616 | tf_op jit(solution)/shard_map/ppermute | solution.py:28
  75.4 7.8 %collective-permute-start.30 = (bf16[1,16,2048]{2,1,0:T(8,128)(2,1)S(1)}, bf16[1,16,2048]{2,1,0:T(8,128)(2,1)S(1)}, u32[]{:S(2)}, u32[]{:S(2)}) collective-permute-start(bf16[1,16,2048]{2,1,0:T(8,128)(2,1)S(1)} %get-tuple-element.21), channel_id=1, source_target_pairs={{0,8},{2,10},{4,12},{6,14},{8,0},{10,2},{12,4},{14,6},{1,9},{3,11}... | collective-permute-start | bytes 196616 | tf_op jit(solution)/shard_map/ppermute | solution.py:28
  76.2 7.0 %collective-permute-start.29 = (bf16[1,16,2048]{2,1,0:T(8,128)(2,1)S(1)}, bf16[1,16,2048]{2,1,0:T(8,128)(2,1)S(1)}, u32[]{:S(2)}, u32[]{:S(2)}) collective-permute-start(bf16[1,16,2048]{2,1,0:T(8,128)(2,1)S(1)} %get-tuple-element.19), channel_id=1, source_target_pairs={{0,4},{2,6},{4,0},{6,2},{8,12},{10,14},{12,8},{14,10},{1,5},{3,7},... | collective-permute-start | bytes 196616 | tf_op jit(solution)/shard_map/ppermute | solution.py:28
  78.8 6.2 %collective-permute-start.27 = (bf16[1,16,2048]{2,1,0:T(8,128)(2,1)S(1)}, bf16[1,16,2048]{2,1,0:T(8,128)(2,1)S(1)}, u32[]{:S(2)}, u32[]{:S(2)}) collective-permute-start(bf16[1,16,2048]{2,1,0:T(8,128)(2,1)S(1)} %get-tuple-element.17), channel_id=1, source_target_pairs={{0,12},{2,14},{4,8},{6,10},{8,4},{10,6},{12,0},{14,2},{1,13},{3,15... | collective-permute-start | bytes 196616 | tf_op jit(solution)/shard_map/ppermute | solution.py:28
  80.0 6.3 %collective-permute-start.26 = (bf16[1,16,2048]{2,1,0:T(8,128)(2,1)S(1)}, bf16[1,16,2048]{2,1,0:T(8,128)(2,1)S(1)}, u32[]{:S(2)}, u32[]{:S(2)}) collective-permute-start(bf16[1,16,2048]{2,1,0:T(8,128)(2,1)S(1)} %get-tuple-element.18), channel_id=1, source_target_pairs={{0,8},{2,10},{4,12},{6,14},{8,0},{10,2},{12,4},{14,6},{1,9},{3,11}... | collective-permute-start | bytes 196616 | tf_op jit(solution)/shard_map/ppermute | solution.py:28
  80.4 5.8 %collective-permute-start.25 = (bf16[1,16,2048]{2,1,0:T(8,128)(2,1)S(1)}, bf16[1,16,2048]{2,1,0:T(8,128)(2,1)S(1)}, u32[]{:S(2)}, u32[]{:S(2)}) collective-permute-start(bf16[1,16,2048]{2,1,0:T(8,128)(2,1)S(1)} %get-tuple-element.16), channel_id=1, source_target_pairs={{0,4},{2,6},{4,0},{6,2},{8,12},{10,14},{12,8},{14,10},{1,5},{3,7},... | collective-permute-start | bytes 196616 | tf_op jit(solution)/shard_map/ppermute | solution.py:28

commit v10 on v9

--- a/solution.py
+++ b/solution.py
@@ -29,10 +29,11 @@
 
 
 def exchange_sum(value, axis):
-    step = 1
-    while step < lax.axis_size(axis):
-        value = value + swap(value, axis, step)
-        step *= 2
+    for stride, radix in levels_of(lax.axis_size(axis)):
+        terms = [value] + [swap(value, axis, t * stride) for t in range(1, radix)]
+        while len(terms) > 1:
+            terms = [terms[i] + terms[i + 1] for i in range(0, len(terms), 2)]
+        value = terms[0]
     return value
 
 
@@ -100,12 +101,9 @@
 
 
 def sketch_kernel(start_ref, slab_ref, *refs):
-    outs, (start_buffer, buffer, start_here, arrived) = refs[:-4], refs[-4:]
-    start = pltpu.make_async_copy(start_ref, start_buffer, start_here)
-    start.start()
+    outs, (buffer, arrived) = refs[:-2], refs[-2:]
     copies = fetch_tiles(slab_ref, buffer, arrived)
-    start.wait()
-    left = start_buffer[...].T
+    left = start_ref[...].T
     for tile, copy in enumerate(copies):
         copy.wait()
         out, inner = divmod(tile * TILE, outs[0].shape[1])
@@ -120,12 +118,13 @@
     return pl.pallas_call(
         sketch_kernel,
         out_shape=[jax.ShapeDtypeStruct((width, cols // chunks), jnp.float32)] * chunks,
-        in_specs=[pl.BlockSpec(memory_space=pl.ANY)] * 2,
+        in_specs=[
+            pl.BlockSpec(memory_space=pltpu.VMEM),
+            pl.BlockSpec(memory_space=pl.ANY),
+        ],
         out_specs=[pl.BlockSpec(memory_space=pltpu.VMEM)] * chunks,
         scratch_shapes=[
-            pltpu.VMEM((rows, width), jnp.bfloat16),
             pltpu.VMEM((cols // TILE, rows, TILE), jnp.bfloat16),
-            pltpu.SemaphoreType.DMA,
             pltpu.SemaphoreType.DMA((cols // TILE,)),
         ],
         compiler_params=pltpu.CompilerParams(vmem_limit_bytes=KERNEL_VMEM),
@@ -160,6 +159,44 @@
     )
 
 
+def gram_kernel(total_cols, mine_ref, other_ref, packed_ref):
+    sketch = (mine_ref[...] + other_ref[...]) / total_cols
+    gram = matmul(sketch.T, sketch)
+    half = gram.shape[0] // 2
+    row = lax.broadcasted_iota(jnp.int32, (half, 2 * half), 0)
+    col = lax.broadcasted_iota(jnp.int32, (half, 2 * half), 1)
+    top, bottom = gram[:half], pltpu.roll(gram[half:], half, 1)
+    packed_ref[:half] = jnp.where(row > col, bottom, top)
+    diagonal = jnp.sum(jnp.where(row == col, bottom, 0.0), axis=0, keepdims=True)
+    packed_ref[half:] = jnp.broadcast_to(diagonal, (8, 2 * half))
+
+
+def unpack_gram(packed):
+    width = packed.shape[1]
+    half = width // 2
+    row = lax.broadcasted_iota(jnp.int32, (half, width), 0)
+    col = lax.broadcasted_iota(jnp.int32, (half, width), 1)
+    square = packed[:half]
+    top = jnp.where(row > col, 0.0, square)
+    lower = jnp.where(row > col, square, jnp.where(row == col, packed[half : half + 1], 0.0))
+    parts = jnp.concatenate([top, pltpu.roll(lower, half, 1)], axis=0)
+    row = lax.broadcasted_iota(jnp.int32, (width, width), 0)
+    col = lax.broadcasted_iota(jnp.int32, (width, width), 1)
+    return jnp.where(row == col, parts, parts + parts.T)
+
+
+def make_gram(mine, other, total_cols):
+    rows, width = mine.shape
+    return pl.pallas_call(
+        functools.partial(gram_kernel, total_cols),
+        out_shape=jax.ShapeDtypeStruct((width // 2 + 8, width), jnp.float32),
+        in_specs=[pl.BlockSpec(memory_space=pltpu.VMEM)] * 2,
+        out_specs=pl.BlockSpec(memory_space=pltpu.VMEM),
+        compiler_params=pltpu.CompilerParams(vmem_limit_bytes=16 * 2**20),
+        name="make_gram",
+    )(mine, other)
+
+
 UPDATES = 4
 LOOSE_UPDATES = 2
 CLOSE = 1e-5
@@ -169,15 +206,16 @@
     total_cols, root_rows, gram_ref, mine_ref, other_ref, slab_ref,
     basis_ref, product_ref, work_ref, inverse_ref, buffer, arrived,
 ):
-    copies = fetch_tiles(slab_ref, buffer, arrived)
-    width = gram_ref.shape[0]
+    fetch = pltpu.make_async_copy(slab_ref, buffer, arrived)
+    fetch.start()
+    width = gram_ref.shape[1]
     row = lax.broadcasted_iota(jnp.int32, (width, width), 0)
     col = lax.broadcasted_iota(jnp.int32, (width, width), 1)
     on_diag = row == col
     unit = jnp.where(on_diag, 1.0, 0.0)
     half = jnp.where(row > col, 1.0, jnp.where(on_diag, 0.5, 0.0))
 
-    gram = gram_ref[...]
+    gram = unpack_gram(gram_ref[...])
     diagonal = jnp.where(on_diag, gram, 0.0)
     down = lax.rsqrt(jnp.sum(diagonal, axis=1, keepdims=True))
     across = lax.rsqrt(jnp.sum(diagonal, axis=0, keepdims=True))
@@ -221,12 +259,15 @@
     high = basis.astype(jnp.bfloat16)
     low = (basis - high.astype(jnp.float32)).astype(jnp.bfloat16)
     pair = jnp.concatenate([high, low], axis=1).T
-    for tile, copy in enumerate(copies):
-        copy.wait()
+    fetch.wait()
+    for start in range(0, buffer.shape[1], TILE):
         both = lax.dot_general(
-            pair, buffer[tile], (((1,), (0,)), ((), ())), preferred_element_type=jnp.float32
-        )
-        product_ref[:, tile * TILE : (tile + 1) * TILE] = both[:width] + both[width:]
+            pair,
+            buffer[:, start : start + TILE],
+            (((1,), (0,)), ((), ())),
+            preferred_element_type=jnp.float32,
+        )
+        product_ref[:, start : start + TILE] = both[:width] + both[width:]
 
 
 def make_basis(gram, mine, other, slab, total_cols, root_rows):
@@ -243,8 +284,8 @@
         scratch_shapes=[
             pltpu.VMEM((width, width), jnp.float32),
             pltpu.VMEM((width, width), jnp.float32),
-            pltpu.VMEM((slab.shape[1] // TILE, rows, TILE), jnp.bfloat16),
-            pltpu.SemaphoreType.DMA((slab.shape[1] // TILE,)),
+            pltpu.VMEM(slab.shape, jnp.bfloat16),
+            pltpu.SemaphoreType.DMA,
         ],
         compiler_params=pltpu.CompilerParams(vmem_limit_bytes=KERNEL_VMEM),
         name="make_basis",
@@ -276,12 +317,7 @@
             preferred_element_type=jnp.float32,
         )
     other_sketch = swap(partial_sketch, "col", 1)
-    sketch = (partial_sketch + other_sketch) / total_cols
-
-    local_gram = lax.dot_general(
-        sketch, sketch, (((0,), (0,)), ((), ())), precision=lax.Precision.HIGHEST
-    )
-    gram = exchange_sum(local_gram, "row")
+    gram = exchange_sum(make_gram(partial_sketch, other_sketch, total_cols), "row")
     basis, local_proj = make_basis(
         gram, partial_sketch, other_sketch, activations, total_cols, root_rows
     )

time: 87.2 us -> 83.7 us (0.960)
  waiting for transfers between devices: 29.9 us -> 27.8 us
  Pallas kernels: 9.28 us -> 8.12 us
    ppermute x32 -> x33, waiting for transfers between devices: 29.9 us -> 27.8 us  [swap(): return lax.ppermute(value, axis, [(i, i ^ distance) for i in range(size)])]
    pallas_call x1, Pallas kernels: 6.15 us -> 4.63 us  [make_basis(): pl.pallas_call(functools.partial(basis_kernel, total_cols, root_rows), ou...]
    ppermute x32 -> x33, starting transfers between devices: 41.6 us -> 41.9 us  [swap(): return lax.ppermute(value, axis, [(i, i ^ distance) for i in range(size)])]
  transfers between devices with their start and end apart: 32 -> 33, of which waited for: 18 -> 19; matrix products, arithmetic and copies ran while one was open for 3% -> 3% of each run, Pallas kernels for 0% -> 0%
where the time goes in v10:
time: 83.7 us; the launch traced here: 83.6 us
  starting transfers between devices  41.9 us (50%)
  waiting for transfers between devices  27.8 us (33%)
  Pallas kernels  8.12 us (10%)
  other arithmetic  1.8 us (2%)
  matrix products  1.74 us (2%)
  local copies, waits for them, and re-layouts  1.17 us (1%)
  between operations  0.97 us (1%)
    ppermute x33, starting transfers between devices, swap(): return lax.ppermute(value, axis, [(i, i ^ distance) for i in range(size)])  41.9 us
    ppermute x33, waiting for transfers between devices, swap(): return lax.ppermute(value, axis, [(i, i ^ distance) for i in range(size)])  27.8 us
    pallas_call x1, Pallas kernels, make_basis(): pl.pallas_call(functools.partial(basis_kernel, total_cols, root_rows), ou...  4.63 us
    pallas_call x1, Pallas kernels, first_product(): pl.pallas_call(sketch_kernel, out_shape=[jax.ShapeDtypeStruct((width, col...  3 us
    dot_general x4, matrix products, per_device(): lax.dot_general(activations[:, span], shared, (((1,), (1,)), ((), ())), p...  1.74 us
  transfers between devices with their start and end apart: 33, of which 19 were waited for; matrix products, arithmetic and copies ran while one was open for 3% of the time, Pallas kernels for 0%

profile of v10, /device:TPU:0, one launch (start us, length us, event | category | flops | bytes accessed | tf_op | source)
XLA Modules:
  0.0 83.6 jit_solution(220517653991395254)
XLA Ops:
  0.7 0.9 %copy-done = bf16[512,128]{1,0:T(8,128)(2,1)S(1)} copy-done((bf16[512,128]{1,0:T(8,128)(2,1)S(1)}, bf16[512,128]{1,0:T(8,128)(2,1)}, u32[]{:S(2)}) %copy-start) | copy-done | bytes 131096
  1.6 3.0 %first_product.1 = (f32[128,1024]{1,0:T(8,128)S(1)}, f32[128,1024]{1,0:T(8,128)S(1)}, f32[128,1024]{1,0:T(8,128)S(1)}, f32[128,1024]{1,0:T(8,128)S(1)}) custom-call(bf16[512,128]{1,0:T(8,128)(2,1)S(1)} %copy-done, bf16[512,4096]{1,0:T(8,128)(2,1)} %slab_ref.3), custom_call_target="tpu_custom_call" | custom-call | flops 536870912 | bytes 4194304 | tf_op jit(solution)/shard_map/first_product/pallas_call | solution.py:118
  4.6 3.1 %collective-permute-start.15 = (bf16[128,512]{1,0:T(8,128)(2,1)S(1)}, bf16[128,512]{1,0:T(8,128)(2,1)S(1)}, u32[]{:S(2)}, u32[]{:S(2)}) collective-permute-start(bf16[128,512]{1,0:T(8,128)(2,1)S(1)} %select_convert_fusion), channel_id=1, source_target_pairs={{0,4},{2,6},{4,0},{6,2},{8,12},{10,14},{12,8},{14,10},{1,5},{3,7},... | collective-permute-start | bytes 393224 | tf_op jit(solution)/shard_map/ppermute | solution.py:28
  7.7 1.6 %collective-permute-start.10 = (bf16[128,512]{1,0:T(8,128)(2,1)S(1)}, bf16[128,512]{1,0:T(8,128)(2,1)S(1)}, u32[]{:S(2)}, u32[]{:S(2)}) collective-permute-start(bf16[128,512]{1,0:T(8,128)(2,1)S(1)} %select_convert_fusion.1), channel_id=1, source_target_pairs={{0,2},{2,0},{4,6},{6,4},{8,10},{10,8},{12,14},{14,12},{1,3},{3,1},... | collective-permute-start | bytes 393224 | tf_op jit(solution)/shard_map/ppermute | solution.py:28
  9.3 0.5 collective-permute-start.5
  10.0 1.6 %collective-permute-done.15 = bf16[128,512]{1,0:T(8,128)(2,1)S(1)} collective-permute-done((bf16[128,512]{1,0:T(8,128)(2,1)S(1)}, bf16[128,512]{1,0:T(8,128)(2,1)S(1)}, u32[]{:S(2)}, u32[]{:S(2)}) %collective-permute-start.15) | collective-permute-done | bytes 131104 | tf_op jit(solution)/shard_map/ppermute | solution.py:28
  11.7 2.4 %collective-permute-start.16 = (bf16[128,256]{1,0:T(8,128)(2,1)S(1)}, bf16[128,256]{1,0:T(8,128)(2,1)S(1)}, u32[]{:S(2)}, u32[]{:S(2)}) collective-permute-start(bf16[128,256]{1,0:T(8,128)(2,1)S(1)} %select_convert_fusion.4), channel_id=1, source_target_pairs={{0,2},{2,0},{4,6},{6,4},{8,10},{10,8},{12,14},{14,12},{1,3},{3,1},... | collective-permute-start | bytes 196616 | tf_op jit(solution)/shard_map/ppermute | solution.py:28
  14.1 1.7 %collective-permute-start.11 = (bf16[128,256]{1,0:T(8,128)(2,1)S(1)}, bf16[128,256]{1,0:T(8,128)(2,1)S(1)}, u32[]{:S(2)}, u32[]{:S(2)}) collective-permute-start(bf16[128,256]{1,0:T(8,128)(2,1)S(1)} %select_convert_fusion.5), channel_id=1, source_target_pairs={{0,4},{2,6},{4,0},{6,2},{8,12},{10,14},{12,8},{14,10},{1,5},{3,7},... | collective-permute-start | bytes 196616 | tf_op jit(solution)/shard_map/ppermute | solution.py:28
  16.0 0.6 collective-permute-start.6
  16.7 1.5 %collective-permute-start.1 = (bf16[128,256]{1,0:T(8,128)(2,1)S(1)}, bf16[128,256]{1,0:T(8,128)(2,1)S(1)}, u32[]{:S(2)}, u32[]{:S(2)}) collective-permute-start(bf16[128,256]{1,0:T(8,128)(2,1)S(1)} %select_convert_fusion.7), channel_id=1, source_target_pairs={{0,4},{2,6},{4,0},{6,2},{8,12},{10,14},{12,8},{14,10},{1,5},{3,7},... | collective-permute-start | bytes 196616 | tf_op jit(solution)/shard_map/ppermute | solution.py:28
  18.2 2.6 %collective-permute-start.17 = (bf16[128,256]{1,0:T(8,128)(2,1)S(1)}, bf16[128,256]{1,0:T(8,128)(2,1)S(1)}, u32[]{:S(2)}, u32[]{:S(2)}) collective-permute-start(bf16[128,256]{1,0:T(8,128)(2,1)S(1)} %fusion.27), channel_id=1, source_target_pairs={{0,8},{2,10},{4,12},{6,14},{8,0},{10,2},{12,4},{14,6},{1,9},{3,11}... | collective-permute-start | bytes 196616 | tf_op jit(solution)/shard_map/ppermute | solution.py:28
  20.9 0.9 %collective-permute-start.12 = (bf16[128,256]{1,0:T(8,128)(2,1)S(1)}, bf16[128,256]{1,0:T(8,128)(2,1)S(1)}, u32[]{:S(2)}, u32[]{:S(2)}) collective-permute-start(bf16[128,256]{1,0:T(8,128)(2,1)S(1)} %fusion.26), channel_id=1, source_target_pairs={{0,8},{2,10},{4,12},{6,14},{8,0},{10,2},{12,4},{14,6},{1,9},{3,11}... | collective-permute-start | bytes 196616 | tf_op jit(solution)/shard_map/ppermute | solution.py:28
  21.8 2.2 %collective-permute-start.7 = (bf16[128,256]{1,0:T(8,128)(2,1)S(1)}, bf16[128,256]{1,0:T(8,128)(2,1)S(1)}, u32[]{:S(2)}, u32[]{:S(2)}) collective-permute-start(bf16[128,256]{1,0:T(8,128)(2,1)S(1)} %fusion.25), channel_id=1, source_target_pairs={{0,8},{2,10},{4,12},{6,14},{8,0},{10,2},{12,4},{14,6},{1,9},{3,11}... | collective-permute-start | bytes 196616 | tf_op jit(solution)/shard_map/ppermute | solution.py:28
  24.0 0.9 %collective-permute-start.2 = (bf16[128,256]{1,0:T(8,128)(2,1)S(1)}, bf16[128,256]{1,0:T(8,128)(2,1)S(1)}, u32[]{:S(2)}, u32[]{:S(2)}) collective-permute-start(bf16[128,256]{1,0:T(8,128)(2,1)S(1)} %fusion.24), channel_id=1, source_target_pairs={{0,8},{2,10},{4,12},{6,14},{8,0},{10,2},{12,4},{14,6},{1,9},{3,11}... | collective-permute-start | bytes 196616 | tf_op jit(solution)/shard_map/ppermute | solution.py:28
  24.9 2.2 %collective-permute-done.17 = bf16[128,256]{1,0:T(8,128)(2,1)S(1)} collective-permute-done((bf16[128,256]{1,0:T(8,128)(2,1)S(1)}, bf16[128,256]{1,0:T(8,128)(2,1)S(1)}, u32[]{:S(2)}, u32[]{:S(2)}) %collective-permute-start.17) | collective-permute-done | bytes 65568 | tf_op jit(solution)/shard_map/ppermute | solution.py:28
  27.1 1.8 %collective-permute-start.18 = (bf16[128,256]{1,0:T(8,128)(2,1)S(1)}, bf16[128,256]{1,0:T(8,128)(2,1)S(1)}, u32[]{:S(2)}, u32[]{:S(2)}) collective-permute-start(bf16[128,256]{1,0:T(8,128)(2,1)S(1)} %multiply_convert_fusion), channel_id=1, source_target_pairs={{0,2},{2,0},{4,6},{6,4},{8,10},{10,8},{12,14},{14,12},{1,3},{3,1},... | collective-permute-start | bytes 196616 | tf_op jit(solution)/shard_map/ppermute | solution.py:28
  28.9 1.1 %collective-permute-done.12 = bf16[128,256]{1,0:T(8,128)(2,1)S(1)} collective-permute-done((bf16[128,256]{1,0:T(8,128)(2,1)S(1)}, bf16[128,256]{1,0:T(8,128)(2,1)S(1)}, u32[]{:S(2)}, u32[]{:S(2)}) %collective-permute-start.12) | collective-permute-done | bytes 65568 | tf_op jit(solution)/shard_map/ppermute | solution.py:28
  30.1 1.0 %collective-permute-done.7 = bf16[128,256]{1,0:T(8,128)(2,1)S(1)} collective-permute-done((bf16[128,256]{1,0:T(8,128)(2,1)S(1)}, bf16[128,256]{1,0:T(8,128)(2,1)S(1)}, u32[]{:S(2)}, u32[]{:S(2)}) %collective-permute-start.7) | collective-permute-done | bytes 65568 | tf_op jit(solution)/shard_map/ppermute | solution.py:28
  31.1 1.2 %collective-permute-start.8 = (bf16[128,256]{1,0:T(8,128)(2,1)S(1)}, bf16[128,256]{1,0:T(8,128)(2,1)S(1)}, u32[]{:S(2)}, u32[]{:S(2)}) collective-permute-start(bf16[128,256]{1,0:T(8,128)(2,1)S(1)} %multiply_convert_fusion.2), channel_id=1, source_target_pairs={{0,2},{2,0},{4,6},{6,4},{8,10},{10,8},{12,14},{14,12},{1,3},{3,1},... | collective-permute-start | bytes 196616 | tf_op jit(solution)/shard_map/ppermute | solution.py:28
  32.3 1.1 %collective-permute-start.3 = (bf16[128,256]{1,0:T(8,128)(2,1)S(1)}, bf16[128,256]{1,0:T(8,128)(2,1)S(1)}, u32[]{:S(2)}, u32[]{:S(2)}) collective-permute-start(bf16[128,256]{1,0:T(8,128)(2,1)S(1)} %multiply_convert_fusion.3), channel_id=1, source_target_pairs={{0,4},{2,6},{4,0},{6,2},{8,12},{10,14},{12,8},{14,10},{1,5},{3,7},... | collective-permute-start | bytes 196616 | tf_op jit(solution)/shard_map/ppermute | solution.py:28
  33.5 1.0 %collective-permute-start.19 = (bf16[128,512]{1,0:T(8,128)(2,1)S(1)}, bf16[128,512]{1,0:T(8,128)(2,1)S(1)}, u32[]{:S(2)}, u32[]{:S(2)}) collective-permute-start(bf16[128,512]{1,0:T(8,128)(2,1)S(1)} %pad_maximum_fusion.4), channel_id=1, source_target_pairs={{0,4},{2,6},{4,0},{6,2},{8,12},{10,14},{12,8},{14,10},{1,5},{3,7},... | collective-permute-start | bytes 393224 | tf_op jit(solution)/shard_map/ppermute | solution.py:28
  34.5 0.5 collective-permute-done.13
  35.1 1.2 %collective-permute-start.14 = (bf16[128,512]{1,0:T(8,128)(2,1)S(1)}, bf16[128,512]{1,0:T(8,128)(2,1)S(1)}, u32[]{:S(2)}, u32[]{:S(2)}) collective-permute-start(bf16[128,512]{1,0:T(8,128)(2,1)S(1)} %pad_maximum_fusion.3), channel_id=1, source_target_pairs={{0,2},{2,0},{4,6},{6,4},{8,10},{10,8},{12,14},{14,12},{1,3},{3,1},... | collective-permute-start | bytes 393224 | tf_op jit(solution)/shard_map/ppermute | solution.py:28
  36.3 0.9 %collective-permute-start.9 = (bf16[128,512]{1,0:T(8,128)(2,1)S(1)}, bf16[128,512]{1,0:T(8,128)(2,1)S(1)}, u32[]{:S(2)}, u32[]{:S(2)}) collective-permute-start(bf16[128,512]{1,0:T(8,128)(2,1)S(1)} %pad_maximum_fusion.2), channel_id=1, source_target_pairs={{0,4},{2,6},{4,0},{6,2},{8,12},{10,14},{12,8},{14,10},{1,5},{3,7},... | collective-permute-start | bytes 393224 | tf_op jit(solution)/shard_map/ppermute | solution.py:28
  37.5 1.1 %collective-permute-start.4 = (bf16[128,512]{1,0:T(8,128)(2,1)S(1)}, bf16[128,512]{1,0:T(8,128)(2,1)S(1)}, u32[]{:S(2)}, u32[]{:S(2)}) collective-permute-start(bf16[128,512]{1,0:T(8,128)(2,1)S(1)} %pad_maximum_fusion.1), channel_id=1, source_target_pairs={{0,2},{2,0},{4,6},{6,4},{8,10},{10,8},{12,14},{14,12},{1,3},{3,1},... | collective-permute-start | bytes 393224 | tf_op jit(solution)/shard_map/ppermute | solution.py:28
  38.5 1.4 %collective-permute-done.19 = bf16[128,512]{1,0:T(8,128)(2,1)S(1)} collective-permute-done((bf16[128,512]{1,0:T(8,128)(2,1)S(1)}, bf16[128,512]{1,0:T(8,128)(2,1)S(1)}, u32[]{:S(2)}, u32[]{:S(2)}) %collective-permute-start.19) | collective-permute-done | bytes 131104 | tf_op jit(solution)/shard_map/ppermute | solution.py:28
  41.4 0.4 fusion.7
  41.9 0.6 collective-permute-done.4
  42.6 0.4 fusion.2.mine_ref
  43.1 1.5 %collective-permute-done.20.other_ref = f32[512,128]{1,0:T(8,128)S(1)} collective-permute-done((f32[512,128]{1,0:T(8,128)S(1)}, f32[512,128]{1,0:T(8,128)S(1)}, u32[]{:S(2)}, u32[]{:S(2)}) %collective-permute-start.20) | collective-permute-done | bytes 262176 | tf_op jit(solution)/shard_map/ppermute | solution.py:28
  44.6 0.5 make_gram.1
  45.1 1.1 %collective-permute-start.21 = (f32[72,128]{1,0:T(8,128)S(1)}, f32[72,128]{1,0:T(8,128)S(1)}, u32[]{:S(2)}, u32[]{:S(2)}) collective-permute-start(f32[72,128]{1,0:T(8,128)S(1)} %make_gram.1), channel_id=1, source_target_pairs={{0,2},{2,0},{4,6},{6,4},{8,10},{10,8},{12,14},{14,12},{1,3},{3,1},... | collective-permute-start | bytes 110600 | tf_op jit(solution)/shard_map/ppermute | solution.py:28
  46.1 3.0 %collective-permute-done.21 = f32[72,128]{1,0:T(8,128)S(1)} collective-permute-done((f32[72,128]{1,0:T(8,128)S(1)}, f32[72,128]{1,0:T(8,128)S(1)}, u32[]{:S(2)}, u32[]{:S(2)}) %collective-permute-start.21) | collective-permute-done | bytes 36896 | tf_op jit(solution)/shard_map/ppermute | solution.py:28
  49.1 1.8 %collective-permute-start.23 = (f32[72,128]{1,0:T(8,128)S(1)}, f32[72,128]{1,0:T(8,128)S(1)}, u32[]{:S(2)}, u32[]{:S(2)}) collective-permute-start(f32[72,128]{1,0:T(8,128)S(1)} %add.127), channel_id=1, source_target_pairs={{0,8},{2,10},{4,12},{6,14},{8,0},{10,2},{12,4},{14,6},{1,9},{3,11}... | collective-permute-start | bytes 110600 | tf_op jit(solution)/shard_map/ppermute | solution.py:28
  51.0 1.6 %collective-permute-start.24 = (f32[72,128]{1,0:T(8,128)S(1)}, f32[72,128]{1,0:T(8,128)S(1)}, u32[]{:S(2)}, u32[]{:S(2)}) collective-permute-start(f32[72,128]{1,0:T(8,128)S(1)} %add.127), channel_id=1, source_target_pairs={{0,12},{2,14},{4,8},{6,10},{8,4},{10,6},{12,0},{14,2},{1,13},{3,15... | collective-permute-start | bytes 110600 | tf_op jit(solution)/shard_map/ppermute | solution.py:28
  52.6 1.5 %collective-permute-done.23 = f32[72,128]{1,0:T(8,128)S(1)} collective-permute-done((f32[72,128]{1,0:T(8,128)S(1)}, f32[72,128]{1,0:T(8,128)S(1)}, u32[]{:S(2)}, u32[]{:S(2)}) %collective-permute-start.23) | collective-permute-done | bytes 36896 | tf_op jit(solution)/shard_map/ppermute | solution.py:28
  54.1 2.7 %collective-permute-done.24 = f32[72,128]{1,0:T(8,128)S(1)} collective-permute-done((f32[72,128]{1,0:T(8,128)S(1)}, f32[72,128]{1,0:T(8,128)S(1)}, u32[]{:S(2)}, u32[]{:S(2)}) %collective-permute-start.24) | collective-permute-done | bytes 36896 | tf_op jit(solution)/shard_map/ppermute | solution.py:28
  56.9 4.6 %make_basis.1 = (f32[512,128]{1,0:T(8,128)}, f32[128,4096]{1,0:T(8,128)S(1)}) custom-call(f32[72,128]{1,0:T(8,128)S(1)} %add_add_fusion.gram_ref, f32[512,128]{1,0:T(8,128)S(1)} %fusion.2.mine_ref, f32[512,128]{1,0:T(8,128)S(1)} %collective-permute-done.20.other_ref, bf16[512,4096]{1,0:T(8,128)(2,1)} %slab_ref.3), custom_call_target="tpu_custom_call" | custom-call | tf_op jit(solution)/shard_map/make_basis/pallas_call | solution.py:275
  61.7 0.9 %collective-permute-start.29 = (bf16[4,16,2048]{2,1,0:T(8,128)(2,1)S(1)}, bf16[4,16,2048]{2,1,0:T(8,128)(2,1)S(1)}, u32[]{:S(2)}, u32[]{:S(2)}) collective-permute-start(bf16[4,16,2048]{2,1,0:T(8,128)(2,1)S(1)} %fusion.11), channel_id=1, source_target_pairs={{0,2},{2,0},{4,6},{6,4},{8,10},{10,8},{12,14},{14,12},{1,3},{3,1},... | collective-permute-start | bytes 786440 | tf_op jit(solution)/shard_map/ppermute | solution.py:28
  62.7 1.2 %collective-permute-start.25 = (bf16[4,16,2048]{2,1,0:T(8,128)(2,1)S(1)}, bf16[4,16,2048]{2,1,0:T(8,128)(2,1)S(1)}, u32[]{:S(2)}, u32[]{:S(2)}) collective-permute-start(bf16[4,16,2048]{2,1,0:T(8,128)(2,1)S(1)} %fusion.10), channel_id=1, source_target_pairs={{0,2},{2,0},{4,6},{6,4},{8,10},{10,8},{12,14},{14,12},{1,3},{3,1},... | collective-permute-start | bytes 786440 | tf_op jit(solution)/shard_map/ppermute | solution.py:28
  63.9 6.7 %collective-permute-done.29 = bf16[4,16,2048]{2,1,0:T(8,128)(2,1)S(1)} collective-permute-done((bf16[4,16,2048]{2,1,0:T(8,128)(2,1)S(1)}, bf16[4,16,2048]{2,1,0:T(8,128)(2,1)S(1)}, u32[]{:S(2)}, u32[]{:S(2)}) %collective-permute-start.29) | collective-permute-done | bytes 262176 | tf_op jit(solution)/shard_map/ppermute | solution.py:28
  70.7 1.9 %collective-permute-start.32 = (bf16[1,16,2048]{2,1,0:T(8,128)(2,1)S(1)}, bf16[1,16,2048]{2,1,0:T(8,128)(2,1)S(1)}, u32[]{:S(2)}, u32[]{:S(2)}) collective-permute-start(bf16[1,16,2048]{2,1,0:T(8,128)(2,1)S(1)} %get-tuple-element.20), channel_id=1, source_target_pairs={{0,12},{2,14},{4,8},{6,10},{8,4},{10,6},{12,0},{14,2},{1,13},{3,15... | collective-permute-start | bytes 196616 | tf_op jit(solution)/shard_map/ppermute | solution.py:28
  72.6 2.6 %collective-permute-start.30 = (bf16[1,16,2048]{2,1,0:T(8,128)(2,1)S(1)}, bf16[1,16,2048]{2,1,0:T(8,128)(2,1)S(1)}, u32[]{:S(2)}, u32[]{:S(2)}) collective-permute-start(bf16[1,16,2048]{2,1,0:T(8,128)(2,1)S(1)} %get-tuple-element.19), channel_id=1, source_target_pairs={{0,4},{2,6},{4,0},{6,2},{8,12},{10,14},{12,8},{14,10},{1,5},{3,7},... | collective-permute-start | bytes 196616 | tf_op jit(solution)/shard_map/ppermute | solution.py:28
  75.3 1.9 %collective-permute-start.28 = (bf16[1,16,2048]{2,1,0:T(8,128)(2,1)S(1)}, bf16[1,16,2048]{2,1,0:T(8,128)(2,1)S(1)}, u32[]{:S(2)}, u32[]{:S(2)}) collective-permute-start(bf16[1,16,2048]{2,1,0:T(8,128)(2,1)S(1)} %get-tuple-element.17), channel_id=1, source_target_pairs={{0,12},{2,14},{4,8},{6,10},{8,4},{10,6},{12,0},{14,2},{1,13},{3,15... | collective-permute-start | bytes 196616 | tf_op jit(solution)/shard_map/ppermute | solution.py:28
  77.4 2.3 %collective-permute-start.26 = (bf16[1,16,2048]{2,1,0:T(8,128)(2,1)S(1)}, bf16[1,16,2048]{2,1,0:T(8,128)(2,1)S(1)}, u32[]{:S(2)}, u32[]{:S(2)}) collective-permute-start(bf16[1,16,2048]{2,1,0:T(8,128)(2,1)S(1)} %get-tuple-element.16), channel_id=1, source_target_pairs={{0,4},{2,6},{4,0},{6,2},{8,12},{10,14},{12,8},{14,10},{1,5},{3,7},... | collective-permute-start | bytes 196616 | tf_op jit(solution)/shard_map/ppermute | solution.py:28
  79.8 1.6 %collective-permute-done.28 = bf16[1,16,2048]{2,1,0:T(8,128)(2,1)S(1)} collective-permute-done((bf16[1,16,2048]{2,1,0:T(8,128)(2,1)S(1)}, bf16[1,16,2048]{2,1,0:T(8,128)(2,1)S(1)}, u32[]{:S(2)}, u32[]{:S(2)}) %collective-permute-start.28) | collective-permute-done | bytes 65568 | tf_op jit(solution)/shard_map/ppermute | solution.py:28
  81.4 1.4 %collective-permute-done.27 = bf16[1,16,2048]{2,1,0:T(8,128)(2,1)S(1)} collective-permute-done((bf16[1,16,2048]{2,1,0:T(8,128)(2,1)S(1)}, bf16[1,16,2048]{2,1,0:T(8,128)(2,1)S(1)}, u32[]{:S(2)}, u32[]{:S(2)}) %collective-permute-start.27) | collective-permute-done | bytes 65568 | tf_op jit(solution)/shard_map/ppermute | solution.py:28
  82.8 0.7 pad_maximum_fusion
  (73 shorter events, 3.6 us)
Async XLA Ops:
  0.6 0.9 %copy-start = (bf16[512,128]{1,0:T(8,128)(2,1)S(1)}, bf16[512,128]{1,0:T(8,128)(2,1)}, u32[]{:S(2)}) copy-start(bf16[512,128]{1,0:T(8,128)(2,1)} %start_ref.1) | copy-start | bytes 393220
  4.6 7.0 %collective-permute-start.15 = (bf16[128,512]{1,0:T(8,128)(2,1)S(1)}, bf16[128,512]{1,0:T(8,128)(2,1)S(1)}, u32[]{:S(2)}, u32[]{:S(2)}) collective-permute-start(bf16[128,512]{1,0:T(8,128)(2,1)S(1)} %select_convert_fusion), channel_id=1, source_target_pairs={{0,4},{2,6},{4,0},{6,2},{8,12},{10,14},{12,8},{14,10},{1,5},{3,7},... | collective-permute-start | bytes 393224 | tf_op jit(solution)/shard_map/ppermute | solution.py:28
  7.7 6.3 %collective-permute-start.10 = (bf16[128,512]{1,0:T(8,128)(2,1)S(1)}, bf16[128,512]{1,0:T(8,128)(2,1)S(1)}, u32[]{:S(2)}, u32[]{:S(2)}) collective-permute-start(bf16[128,512]{1,0:T(8,128)(2,1)S(1)} %select_convert_fusion.1), channel_id=1, source_target_pairs={{0,2},{2,0},{4,6},{6,4},{8,10},{10,8},{12,14},{14,12},{1,3},{3,1},... | collective-permute-start | bytes 393224 | tf_op jit(solution)/shard_map/ppermute | solution.py:28
  9.3 6.6 %collective-permute-start.5 = (bf16[128,512]{1,0:T(8,128)(2,1)S(1)}, bf16[128,512]{1,0:T(8,128)(2,1)S(1)}, u32[]{:S(2)}, u32[]{:S(2)}) collective-permute-start(bf16[128,512]{1,0:T(8,128)(2,1)S(1)} %select_convert_fusion.2), channel_id=1, source_target_pairs={{0,4},{2,6},{4,0},{6,2},{8,12},{10,14},{12,8},{14,10},{1,5},{3,7},... | collective-permute-start | bytes 393224 | tf_op jit(solution)/shard_map/ppermute | solution.py:28
  9.8 6.7 %collective-permute-start = (bf16[128,512]{1,0:T(8,128)(2,1)S(1)}, bf16[128,512]{1,0:T(8,128)(2,1)S(1)}, u32[]{:S(2)}, u32[]{:S(2)}) collective-permute-start(bf16[128,512]{1,0:T(8,128)(2,1)S(1)} %select_convert_fusion.3), channel_id=1, source_target_pairs={{0,2},{2,0},{4,6},{6,4},{8,10},{10,8},{12,14},{14,12},{1,3},{3,1},... | collective-permute-start | bytes 393224 | tf_op jit(solution)/shard_map/ppermute | solution.py:28
  11.7 6.5 %collective-permute-start.16 = (bf16[128,256]{1,0:T(8,128)(2,1)S(1)}, bf16[128,256]{1,0:T(8,128)(2,1)S(1)}, u32[]{:S(2)}, u32[]{:S(2)}) collective-permute-start(bf16[128,256]{1,0:T(8,128)(2,1)S(1)} %select_convert_fusion.4), channel_id=1, source_target_pairs={{0,2},{2,0},{4,6},{6,4},{8,10},{10,8},{12,14},{14,12},{1,3},{3,1},... | collective-permute-start | bytes 196616 | tf_op jit(solution)/shard_map/ppermute | solution.py:28
  14.1 25.9 %copy-start.1 = (bf16[512,4096]{1,0:T(8,128)(2,1)S(1)}, bf16[512,4096]{1,0:T(8,128)(2,1)}, u32[]{:S(2)}) copy-start(bf16[512,4096]{1,0:T(8,128)(2,1)} %slab_ref.3) | copy-start | bytes 12582916
  14.1 6.7 %collective-permute-start.11 = (bf16[128,256]{1,0:T(8,128)(2,1)S(1)}, bf16[128,256]{1,0:T(8,128)(2,1)S(1)}, u32[]{:S(2)}, u32[]{:S(2)}) collective-permute-start(bf16[128,256]{1,0:T(8,128)(2,1)S(1)} %select_convert_fusion.5), channel_id=1, source_target_pairs={{0,4},{2,6},{4,0},{6,2},{8,12},{10,14},{12,8},{14,10},{1,5},{3,7},... | collective-permute-start | bytes 196616 | tf_op jit(solution)/shard_map/ppermute | solution.py:28
  16.0 5.8 %collective-permute-start.6 = (bf16[128,256]{1,0:T(8,128)(2,1)S(1)}, bf16[128,256]{1,0:T(8,128)(2,1)S(1)}, u32[]{:S(2)}, u32[]{:S(2)}) collective-permute-start(bf16[128,256]{1,0:T(8,128)(2,1)S(1)} %select_convert_fusion.6), channel_id=1, source_target_pairs={{0,2},{2,0},{4,6},{6,4},{8,10},{10,8},{12,14},{14,12},{1,3},{3,1},... | collective-permute-start | bytes 196616 | tf_op jit(solution)/shard_map/ppermute | solution.py:28
  16.7 7.3 %collective-permute-start.1 = (bf16[128,256]{1,0:T(8,128)(2,1)S(1)}, bf16[128,256]{1,0:T(8,128)(2,1)S(1)}, u32[]{:S(2)}, u32[]{:S(2)}) collective-permute-start(bf16[128,256]{1,0:T(8,128)(2,1)S(1)} %select_convert_fusion.7), channel_id=1, source_target_pairs={{0,4},{2,6},{4,0},{6,2},{8,12},{10,14},{12,8},{14,10},{1,5},{3,7},... | collective-permute-start | bytes 196616 | tf_op jit(solution)/shard_map/ppermute | solution.py:28
  18.2 8.8 %collective-permute-start.17 = (bf16[128,256]{1,0:T(8,128)(2,1)S(1)}, bf16[128,256]{1,0:T(8,128)(2,1)S(1)}, u32[]{:S(2)}, u32[]{:S(2)}) collective-permute-start(bf16[128,256]{1,0:T(8,128)(2,1)S(1)} %fusion.27), channel_id=1, source_target_pairs={{0,8},{2,10},{4,12},{6,14},{8,0},{10,2},{12,4},{14,6},{1,9},{3,11}... | collective-permute-start | bytes 196616 | tf_op jit(solution)/shard_map/ppermute | solution.py:28
  20.9 9.1 %collective-permute-start.12 = (bf16[128,256]{1,0:T(8,128)(2,1)S(1)}, bf16[128,256]{1,0:T(8,128)(2,1)S(1)}, u32[]{:S(2)}, u32[]{:S(2)}) collective-permute-start(bf16[128,256]{1,0:T(8,128)(2,1)S(1)} %fusion.26), channel_id=1, source_target_pairs={{0,8},{2,10},{4,12},{6,14},{8,0},{10,2},{12,4},{14,6},{1,9},{3,11}... | collective-permute-start | bytes 196616 | tf_op jit(solution)/shard_map/ppermute | solution.py:28
  21.8 9.3 %collective-permute-start.7 = (bf16[128,256]{1,0:T(8,128)(2,1)S(1)}, bf16[128,256]{1,0:T(8,128)(2,1)S(1)}, u32[]{:S(2)}, u32[]{:S(2)}) collective-permute-start(bf16[128,256]{1,0:T(8,128)(2,1)S(1)} %fusion.25), channel_id=1, source_target_pairs={{0,8},{2,10},{4,12},{6,14},{8,0},{10,2},{12,4},{14,6},{1,9},{3,11}... | collective-permute-start | bytes 196616 | tf_op jit(solution)/shard_map/ppermute | solution.py:28
  24.0 8.3 %collective-permute-start.2 = (bf16[128,256]{1,0:T(8,128)(2,1)S(1)}, bf16[128,256]{1,0:T(8,128)(2,1)S(1)}, u32[]{:S(2)}, u32[]{:S(2)}) collective-permute-start(bf16[128,256]{1,0:T(8,128)(2,1)S(1)} %fusion.24), channel_id=1, source_target_pairs={{0,8},{2,10},{4,12},{6,14},{8,0},{10,2},{12,4},{14,6},{1,9},{3,11}... | collective-permute-start | bytes 196616 | tf_op jit(solution)/shard_map/ppermute | solution.py:28
  27.1 6.4 %collective-permute-start.18 = (bf16[128,256]{1,0:T(8,128)(2,1)S(1)}, bf16[128,256]{1,0:T(8,128)(2,1)S(1)}, u32[]{:S(2)}, u32[]{:S(2)}) collective-permute-start(bf16[128,256]{1,0:T(8,128)(2,1)S(1)} %multiply_convert_fusion), channel_id=1, source_target_pairs={{0,2},{2,0},{4,6},{6,4},{8,10},{10,8},{12,14},{14,12},{1,3},{3,1},... | collective-permute-start | bytes 196616 | tf_op jit(solution)/shard_map/ppermute | solution.py:28
  30.0 5.0 %collective-permute-start.13 = (bf16[128,256]{1,0:T(8,128)(2,1)S(1)}, bf16[128,256]{1,0:T(8,128)(2,1)S(1)}, u32[]{:S(2)}, u32[]{:S(2)}) collective-permute-start(bf16[128,256]{1,0:T(8,128)(2,1)S(1)} %multiply_convert_fusion.1), channel_id=1, source_target_pairs={{0,4},{2,6},{4,0},{6,2},{8,12},{10,14},{12,8},{14,10},{1,5},{3,7},... | collective-permute-start | bytes 196616 | tf_op jit(solution)/shard_map/ppermute | solution.py:28
  31.1 5.1 %collective-permute-start.8 = (bf16[128,256]{1,0:T(8,128)(2,1)S(1)}, bf16[128,256]{1,0:T(8,128)(2,1)S(1)}, u32[]{:S(2)}, u32[]{:S(2)}) collective-permute-start(bf16[128,256]{1,0:T(8,128)(2,1)S(1)} %multiply_convert_fusion.2), channel_id=1, source_target_pairs={{0,2},{2,0},{4,6},{6,4},{8,10},{10,8},{12,14},{14,12},{1,3},{3,1},... | collective-permute-start | bytes 196616 | tf_op jit(solution)/shard_map/ppermute | solution.py:28
  32.3 5.1 %collective-permute-start.3 = (bf16[128,256]{1,0:T(8,128)(2,1)S(1)}, bf16[128,256]{1,0:T(8,128)(2,1)S(1)}, u32[]{:S(2)}, u32[]{:S(2)}) collective-permute-start(bf16[128,256]{1,0:T(8,128)(2,1)S(1)} %multiply_convert_fusion.3), channel_id=1, source_target_pairs={{0,4},{2,6},{4,0},{6,2},{8,12},{10,14},{12,8},{14,10},{1,5},{3,7},... | collective-permute-start | bytes 196616 | tf_op jit(solution)/shard_map/ppermute | solution.py:28
  33.5 6.4 %collective-permute-start.19 = (bf16[128,512]{1,0:T(8,128)(2,1)S(1)}, bf16[128,512]{1,0:T(8,128)(2,1)S(1)}, u32[]{:S(2)}, u32[]{:S(2)}) collective-permute-start(bf16[128,512]{1,0:T(8,128)(2,1)S(1)} %pad_maximum_fusion.4), channel_id=1, source_target_pairs={{0,4},{2,6},{4,0},{6,2},{8,12},{10,14},{12,8},{14,10},{1,5},{3,7},... | collective-permute-start | bytes 393224 | tf_op jit(solution)/shard_map/ppermute | solution.py:28
  35.1 5.6 %collective-permute-start.14 = (bf16[128,512]{1,0:T(8,128)(2,1)S(1)}, bf16[128,512]{1,0:T(8,128)(2,1)S(1)}, u32[]{:S(2)}, u32[]{:S(2)}) collective-permute-start(bf16[128,512]{1,0:T(8,128)(2,1)S(1)} %pad_maximum_fusion.3), channel_id=1, source_target_pairs={{0,2},{2,0},{4,6},{6,4},{8,10},{10,8},{12,14},{14,12},{1,3},{3,1},... | collective-permute-start | bytes 393224 | tf_op jit(solution)/shard_map/ppermute | solution.py:28
  36.3 5.0 %collective-permute-start.9 = (bf16[128,512]{1,0:T(8,128)(2,1)S(1)}, bf16[128,512]{1,0:T(8,128)(2,1)S(1)}, u32[]{:S(2)}, u32[]{:S(2)}) collective-permute-start(bf16[128,512]{1,0:T(8,128)(2,1)S(1)} %pad_maximum_fusion.2), channel_id=1, source_target_pairs={{0,4},{2,6},{4,0},{6,2},{8,12},{10,14},{12,8},{14,10},{1,5},{3,7},... | collective-permute-start | bytes 393224 | tf_op jit(solution)/shard_map/ppermute | solution.py:28
  37.5 5.0 %collective-permute-start.4 = (bf16[128,512]{1,0:T(8,128)(2,1)S(1)}, bf16[128,512]{1,0:T(8,128)(2,1)S(1)}, u32[]{:S(2)}, u32[]{:S(2)}) collective-permute-start(bf16[128,512]{1,0:T(8,128)(2,1)S(1)} %pad_maximum_fusion.1), channel_id=1, source_target_pairs={{0,2},{2,0},{4,6},{6,4},{8,10},{10,8},{12,14},{14,12},{1,3},{3,1},... | collective-permute-start | bytes 393224 | tf_op jit(solution)/shard_map/ppermute | solution.py:28
  43.0 1.6 %collective-permute-start.20 = (f32[512,128]{1,0:T(8,128)S(1)}, f32[512,128]{1,0:T(8,128)S(1)}, u32[]{:S(2)}, u32[]{:S(2)}) collective-permute-start(f32[512,128]{1,0:T(8,128)S(1)} %fusion.2.mine_ref), channel_id=1, source_target_pairs={{0,1},{1,0},{2,3},{3,2},{4,5},{5,4},{6,7},{7,6},{8,9},{9,8},{10,11... | collective-permute-start | bytes 786440 | tf_op jit(solution)/shard_map/ppermute | solution.py:28
  45.1 4.0 %collective-permute-start.21 = (f32[72,128]{1,0:T(8,128)S(1)}, f32[72,128]{1,0:T(8,128)S(1)}, u32[]{:S(2)}, u32[]{:S(2)}) collective-permute-start(f32[72,128]{1,0:T(8,128)S(1)} %make_gram.1), channel_id=1, source_target_pairs={{0,2},{2,0},{4,6},{6,4},{8,10},{10,8},{12,14},{14,12},{1,3},{3,1},... | collective-permute-start | bytes 110600 | tf_op jit(solution)/shard_map/ppermute | solution.py:28
  49.1 5.0 %collective-permute-start.23 = (f32[72,128]{1,0:T(8,128)S(1)}, f32[72,128]{1,0:T(8,128)S(1)}, u32[]{:S(2)}, u32[]{:S(2)}) collective-permute-start(f32[72,128]{1,0:T(8,128)S(1)} %add.127), channel_id=1, source_target_pairs={{0,8},{2,10},{4,12},{6,14},{8,0},{10,2},{12,4},{14,6},{1,9},{3,11}... | collective-permute-start | bytes 110600 | tf_op jit(solution)/shard_map/ppermute | solution.py:28
  51.0 5.9 %collective-permute-start.24 = (f32[72,128]{1,0:T(8,128)S(1)}, f32[72,128]{1,0:T(8,128)S(1)}, u32[]{:S(2)}, u32[]{:S(2)}) collective-permute-start(f32[72,128]{1,0:T(8,128)S(1)} %add.127), channel_id=1, source_target_pairs={{0,12},{2,14},{4,8},{6,10},{8,4},{10,6},{12,0},{14,2},{1,13},{3,15... | collective-permute-start | bytes 110600 | tf_op jit(solution)/shard_map/ppermute | solution.py:28
  52.5 4.4 %collective-permute-start.22 = (f32[72,128]{1,0:T(8,128)S(1)}, f32[72,128]{1,0:T(8,128)S(1)}, u32[]{:S(2)}, u32[]{:S(2)}) collective-permute-start(f32[72,128]{1,0:T(8,128)S(1)} %add.127), channel_id=1, source_target_pairs={{0,4},{2,6},{4,0},{6,2},{8,12},{10,14},{12,8},{14,10},{1,5},{3,7},... | collective-permute-start | bytes 110600 | tf_op jit(solution)/shard_map/ppermute | solution.py:28
  61.7 8.9 %collective-permute-start.29 = (bf16[4,16,2048]{2,1,0:T(8,128)(2,1)S(1)}, bf16[4,16,2048]{2,1,0:T(8,128)(2,1)S(1)}, u32[]{:S(2)}, u32[]{:S(2)}) collective-permute-start(bf16[4,16,2048]{2,1,0:T(8,128)(2,1)S(1)} %fusion.11), channel_id=1, source_target_pairs={{0,2},{2,0},{4,6},{6,4},{8,10},{10,8},{12,14},{14,12},{1,3},{3,1},... | collective-permute-start | bytes 786440 | tf_op jit(solution)/shard_map/ppermute | solution.py:28
  62.7 12.4 %collective-permute-start.25 = (bf16[4,16,2048]{2,1,0:T(8,128)(2,1)S(1)}, bf16[4,16,2048]{2,1,0:T(8,128)(2,1)S(1)}, u32[]{:S(2)}, u32[]{:S(2)}) collective-permute-start(bf16[4,16,2048]{2,1,0:T(8,128)(2,1)S(1)} %fusion.10), channel_id=1, source_target_pairs={{0,2},{2,0},{4,6},{6,4},{8,10},{10,8},{12,14},{14,12},{1,3},{3,1},... | collective-permute-start | bytes 786440 | tf_op jit(solution)/shard_map/ppermute | solution.py:28
  70.7 6.7 %collective-permute-start.32 = (bf16[1,16,2048]{2,1,0:T(8,128)(2,1)S(1)}, bf16[1,16,2048]{2,1,0:T(8,128)(2,1)S(1)}, u32[]{:S(2)}, u32[]{:S(2)}) collective-permute-start(bf16[1,16,2048]{2,1,0:T(8,128)(2,1)S(1)} %get-tuple-element.20), channel_id=1, source_target_pairs={{0,12},{2,14},{4,8},{6,10},{8,4},{10,6},{12,0},{14,2},{1,13},{3,15... | collective-permute-start | bytes 196616 | tf_op jit(solution)/shard_map/ppermute | solution.py:28
  72.6 7.2 %collective-permute-start.31 = (bf16[1,16,2048]{2,1,0:T(8,128)(2,1)S(1)}, bf16[1,16,2048]{2,1,0:T(8,128)(2,1)S(1)}, u32[]{:S(2)}, u32[]{:S(2)}) collective-permute-start(bf16[1,16,2048]{2,1,0:T(8,128)(2,1)S(1)} %get-tuple-element.21), channel_id=1, source_target_pairs={{0,8},{2,10},{4,12},{6,14},{8,0},{10,2},{12,4},{14,6},{1,9},{3,11}... | collective-permute-start | bytes 196616 | tf_op jit(solution)/shard_map/ppermute | solution.py:28
  72.6 7.2 %collective-permute-start.30 = (bf16[1,16,2048]{2,1,0:T(8,128)(2,1)S(1)}, bf16[1,16,2048]{2,1,0:T(8,128)(2,1)S(1)}, u32[]{:S(2)}, u32[]{:S(2)}) collective-permute-start(bf16[1,16,2048]{2,1,0:T(8,128)(2,1)S(1)} %get-tuple-element.19), channel_id=1, source_target_pairs={{0,4},{2,6},{4,0},{6,2},{8,12},{10,14},{12,8},{14,10},{1,5},{3,7},... | collective-permute-start | bytes 196616 | tf_op jit(solution)/shard_map/ppermute | solution.py:28
  75.3 6.1 %collective-permute-start.28 = (bf16[1,16,2048]{2,1,0:T(8,128)(2,1)S(1)}, bf16[1,16,2048]{2,1,0:T(8,128)(2,1)S(1)}, u32[]{:S(2)}, u32[]{:S(2)}) collective-permute-start(bf16[1,16,2048]{2,1,0:T(8,128)(2,1)S(1)} %get-tuple-element.17), channel_id=1, source_target_pairs={{0,12},{2,14},{4,8},{6,10},{8,4},{10,6},{12,0},{14,2},{1,13},{3,15... | collective-permute-start | bytes 196616 | tf_op jit(solution)/shard_map/ppermute | solution.py:28
  77.1 5.7 %collective-permute-start.27 = (bf16[1,16,2048]{2,1,0:T(8,128)(2,1)S(1)}, bf16[1,16,2048]{2,1,0:T(8,128)(2,1)S(1)}, u32[]{:S(2)}, u32[]{:S(2)}) collective-permute-start(bf16[1,16,2048]{2,1,0:T(8,128)(2,1)S(1)} %get-tuple-element.18), channel_id=1, source_target_pairs={{0,8},{2,10},{4,12},{6,14},{8,0},{10,2},{12,4},{14,6},{1,9},{3,11}... | collective-permute-start | bytes 196616 | tf_op jit(solution)/shard_map/ppermute | solution.py:28
  77.4 5.4 %collective-permute-start.26 = (bf16[1,16,2048]{2,1,0:T(8,128)(2,1)S(1)}, bf16[1,16,2048]{2,1,0:T(8,128)(2,1)S(1)}, u32[]{:S(2)}, u32[]{:S(2)}) collective-permute-start(bf16[1,16,2048]{2,1,0:T(8,128)(2,1)S(1)} %get-tuple-element.16), channel_id=1, source_target_pairs={{0,4},{2,6},{4,0},{6,2},{8,12},{10,14},{12,8},{14,10},{1,5},{3,7},... | collective-permute-start | bytes 196616 | tf_op jit(solution)/shard_map/ppermute | solution.py:28

commit v11 on v10

--- a/solution.py
+++ b/solution.py
@@ -8,7 +8,7 @@
 from jax.experimental.pallas import tpu as pltpu
 from jax.sharding import PartitionSpec as P
 
-SKETCH_CHUNKS = 4
+SKETCH_CHUNKS = 2
 CHUNKS = 2
 TILE = 512
 KERNEL_VMEM = 50 * 2**20
@@ -58,34 +58,45 @@
     return blocks[0]
 
 
-def bit_of(axis, bit):
-    return lax.rem(lax.div(lax.axis_index(axis), 1 << bit), 2)
-
-
-def sum_and_share(value, axis, order, scale):
-    for bit in order[:-1]:
-        upper = bit_of(axis, bit) == 1
+def orders_of(size):
+    bits = list(range((size - 1).bit_length()))
+    return [bits, [bits[1], bits[0]] + bits[2:] if len(bits) > 2 else bits]
+
+
+def core_swap(value, bits):
+    rows, cores = lax.axis_size("row"), lax.axis_size("col")
+    pairs = [
+        (row * cores + core, (row ^ (1 << bits[core % 2])) * cores + core)
+        for row in range(rows)
+        for core in range(cores)
+    ]
+    return lax.ppermute(value, ("row", "col"), pairs)
+
+
+def core_upper(bits):
+    odd = lax.rem(lax.axis_index("col"), 2) == 1
+    weight = jnp.where(odd, 1 << bits[1], 1 << bits[0])
+    return jnp.bitwise_and(lax.axis_index("row"), weight) != 0
+
+
+def sum_and_share(value, scale):
+    steps = list(zip(*orders_of(lax.axis_size("row"))))
+    for bits in steps[:-1]:
+        upper = core_upper(bits)
         half = value.shape[1] // 2
         low, high = value[:, :half], value[:, half:]
         send = jnp.where(upper, low, high).astype(jnp.bfloat16)
-        landed = swap(send, axis, 1 << bit)
+        landed = core_swap(send, bits)
         value = jnp.where(upper, high, low) + landed.astype(jnp.float32)
-    landed = swap(value.astype(jnp.bfloat16), axis, 1 << order[-1])
+    landed = core_swap(value.astype(jnp.bfloat16), steps[-1])
     block = ((value + landed.astype(jnp.float32)) * scale).astype(jnp.bfloat16)
-    for bit in reversed(order[:-1]):
-        upper = bit_of(axis, bit) == 1
-        other = swap(block, axis, 1 << bit)
+    for bits in reversed(steps[:-1]):
+        upper = core_upper(bits)
+        other = core_swap(block, bits)
         block = jnp.concatenate(
             [jnp.where(upper, other, block), jnp.where(upper, block, other)], axis=1
         )
     return block
-
-
-def orders_of(axis):
-    bits = list(range((lax.axis_size(axis) - 1).bit_length()))
-    if len(bits) < 3:
-        return [bits, bits]
-    return [bits, [bits[1], bits[0]] + bits[2:]]
 
 
 def fetch_tiles(slab_ref, buffer, arrived):
@@ -305,11 +316,10 @@
 
     local_cols = first_product(start_sketch, activations, SKETCH_CHUNKS)
     partial_sketch = 0.0
-    orders = orders_of("row")
     step = cols_here // SKETCH_CHUNKS
     for c in range(SKETCH_CHUNKS):
         span = slice(c * step, (c + 1) * step)
-        shared = sum_and_share(local_cols[c], "row", orders[c % 2], 1.0 / root_rows)
+        shared = sum_and_share(local_cols[c], 1.0 / root_rows)
         partial_sketch = partial_sketch + lax.dot_general(
             activations[:, span],
             shared,

time: 83.7 us -> 86.8 us (1.037)
  waiting for transfers between devices: 27.8 us -> 38 us
  starting transfers between devices: 41.9 us -> 35.2 us
    ppermute x33 -> x13, starting transfers between devices: 41.9 us -> 16.4 us  [swap(): return lax.ppermute(value, axis, [(i, i ^ distance) for i in range(size)])]
    ppermute x0 -> x10, waiting for transfers between devices: none -> 20.4 us  [core_swap(): return lax.ppermute(value, ('row', 'col'), pairs)]
    ppermute x0 -> x10, starting transfers between devices: none -> 18.9 us  [core_swap(): return lax.ppermute(value, ('row', 'col'), pairs)]
    ppermute x33 -> x13, waiting for transfers between devices: 27.8 us -> 17.6 us  [swap(): return lax.ppermute(value, axis, [(i, i ^ distance) for i in range(size)])]
    dot_general x4 -> x2, matrix products: 1.74 us -> 1.44 us  [per_device(): lax.dot_general(activations[:, span], shared, (((1,), (1,)), ((), ())), p...]
  transfers between devices with their start and end apart: 33 -> 23, of which waited for: 19 -> 18; matrix products, arithmetic and copies ran while one was open for 3% -> 2% of each run, Pallas kernels for 0% -> 0%
where the time goes in v11:
time: 86.8 us; the launch traced here: 86.7 us
  waiting for transfers between devices  38 us (44%)
  starting transfers between devices  35.2 us (41%)
  Pallas kernels  8.13 us (9%)
  other arithmetic  1.81 us (2%)
  matrix products  1.44 us (2%)
  local copies, waits for them, and re-layouts  1.17 us (1%)
  between operations  0.87 us (1%)
    ppermute x10, waiting for transfers between devices, core_swap(): return lax.ppermute(value, ('row', 'col'), pairs)  20.4 us
    ppermute x10, starting transfers between devices, core_swap(): return lax.ppermute(value, ('row', 'col'), pairs)  18.9 us
    ppermute x13, waiting for transfers between devices, swap(): return lax.ppermute(value, axis, [(i, i ^ distance) for i in range(size)])  17.6 us
    ppermute x13, starting transfers between devices, swap(): return lax.ppermute(value, axis, [(i, i ^ distance) for i in range(size)])  16.4 us
    pallas_call x1, Pallas kernels, make_basis(): pl.pallas_call(functools.partial(basis_kernel, total_cols, root_rows), ou...  4.63 us
    pallas_call x1, Pallas kernels, first_product(): pl.pallas_call(sketch_kernel, out_shape=[jax.ShapeDtypeStruct((width, col...  3 us
  transfers between devices with their start and end apart: 23, of which 18 were waited for; matrix products, arithmetic and copies ran while one was open for 2% of the time, Pallas kernels for 0%

profile of v11, /device:TPU:0, one launch (start us, length us, event | category | flops | bytes accessed | tf_op | source)
XLA Modules:
  0.0 86.7 jit_solution(14967244450852338094)
XLA Ops:
  0.7 0.9 %copy-done = bf16[512,128]{1,0:T(8,128)(2,1)S(1)} copy-done((bf16[512,128]{1,0:T(8,128)(2,1)S(1)}, bf16[512,128]{1,0:T(8,128)(2,1)}, u32[]{:S(2)}) %copy-start) | copy-done | bytes 131096
  1.5 3.0 %first_product.1 = (f32[128,2048]{1,0:T(8,128)S(1)}, f32[128,2048]{1,0:T(8,128)S(1)}) custom-call(bf16[512,128]{1,0:T(8,128)(2,1)S(1)} %copy-done, bf16[512,4096]{1,0:T(8,128)(2,1)} %slab_ref.3), custom_call_target="tpu_custom_call" | custom-call | flops 536870912 | bytes 4194304 | tf_op jit(solution)/shard_map/first_product/pallas_call | solution.py:129
  4.6 3.0 %collective-permute-start.5 = (bf16[128,1024]{1,0:T(8,128)(2,1)S(1)}, bf16[128,1024]{1,0:T(8,128)(2,1)S(1)}, u32[]{:S(2)}, u32[]{:S(2)}) collective-permute-start(bf16[128,1024]{1,0:T(8,128)(2,1)S(1)} %select_convert_fusion), channel_id=1, source_target_pairs={{0,2},{1,5},{2,0},{3,7},{4,6},{5,1},{6,4},{7,3},{8,10},{9,13},{10,... | collective-permute-start | bytes 786440 | tf_op jit(solution)/shard_map/ppermute | solution.py:73
  7.8 4.2 %collective-permute-done.5 = bf16[128,1024]{1,0:T(8,128)(2,1)S(1)} collective-permute-done((bf16[128,1024]{1,0:T(8,128)(2,1)S(1)}, bf16[128,1024]{1,0:T(8,128)(2,1)S(1)}, u32[]{:S(2)}, u32[]{:S(2)}) %collective-permute-start.5) | collective-permute-done | bytes 262176 | tf_op jit(solution)/shard_map/ppermute | solution.py:73
  12.1 2.2 %collective-permute-start.6 = (bf16[128,512]{1,0:T(8,128)(2,1)S(1)}, bf16[128,512]{1,0:T(8,128)(2,1)S(1)}, u32[]{:S(2)}, u32[]{:S(2)}) collective-permute-start(bf16[128,512]{1,0:T(8,128)(2,1)S(1)} %select_convert_fusion.2), channel_id=1, source_target_pairs={{0,4},{1,3},{2,6},{3,1},{4,0},{5,7},{6,2},{7,5},{8,12},{9,11},{10,... | collective-permute-start | bytes 393224 | tf_op jit(solution)/shard_map/ppermute | solution.py:73
  14.3 1.1 %collective-permute-done = bf16[128,1024]{1,0:T(8,128)(2,1)S(1)} collective-permute-done((bf16[128,1024]{1,0:T(8,128)(2,1)S(1)}, bf16[128,1024]{1,0:T(8,128)(2,1)S(1)}, u32[]{:S(2)}, u32[]{:S(2)}) %collective-permute-start) | collective-permute-done | bytes 262176 | tf_op jit(solution)/shard_map/ppermute | solution.py:73
  15.5 2.5 %collective-permute-start.1 = (bf16[128,512]{1,0:T(8,128)(2,1)S(1)}, bf16[128,512]{1,0:T(8,128)(2,1)S(1)}, u32[]{:S(2)}, u32[]{:S(2)}) collective-permute-start(bf16[128,512]{1,0:T(8,128)(2,1)S(1)} %select_convert_fusion.3), channel_id=1, source_target_pairs={{0,4},{1,3},{2,6},{3,1},{4,0},{5,7},{6,2},{7,5},{8,12},{9,11},{10,... | collective-permute-start | bytes 393224 | tf_op jit(solution)/shard_map/ppermute | solution.py:73
  18.1 2.6 %collective-permute-start.7 = (bf16[128,512]{1,0:T(8,128)(2,1)S(1)}, bf16[128,512]{1,0:T(8,128)(2,1)S(1)}, u32[]{:S(2)}, u32[]{:S(2)}) collective-permute-start(bf16[128,512]{1,0:T(8,128)(2,1)S(1)} %fusion.19), channel_id=1, source_target_pairs={{0,8},{1,9},{2,10},{3,11},{4,12},{5,13},{6,14},{7,15},{8,0},{9,1},... | collective-permute-start | bytes 393224 | tf_op jit(solution)/shard_map/ppermute | solution.py:73
  20.8 1.4 %collective-permute-done.1 = bf16[128,512]{1,0:T(8,128)(2,1)S(1)} collective-permute-done((bf16[128,512]{1,0:T(8,128)(2,1)S(1)}, bf16[128,512]{1,0:T(8,128)(2,1)S(1)}, u32[]{:S(2)}, u32[]{:S(2)}) %collective-permute-start.1) | collective-permute-done | bytes 131104 | tf_op jit(solution)/shard_map/ppermute | solution.py:73
  22.2 3.1 %collective-permute-start.2 = (bf16[128,512]{1,0:T(8,128)(2,1)S(1)}, bf16[128,512]{1,0:T(8,128)(2,1)S(1)}, u32[]{:S(2)}, u32[]{:S(2)}) collective-permute-start(bf16[128,512]{1,0:T(8,128)(2,1)S(1)} %fusion.18), channel_id=1, source_target_pairs={{0,8},{1,9},{2,10},{3,11},{4,12},{5,13},{6,14},{7,15},{8,0},{9,1},... | collective-permute-start | bytes 393224 | tf_op jit(solution)/shard_map/ppermute | solution.py:73
  25.3 5.0 %collective-permute-done.7 = bf16[128,512]{1,0:T(8,128)(2,1)S(1)} collective-permute-done((bf16[128,512]{1,0:T(8,128)(2,1)S(1)}, bf16[128,512]{1,0:T(8,128)(2,1)S(1)}, u32[]{:S(2)}, u32[]{:S(2)}) %collective-permute-start.7) | collective-permute-done | bytes 131104 | tf_op jit(solution)/shard_map/ppermute | solution.py:73
  30.3 0.4 collective-permute-start.8
  30.7 1.0 %collective-permute-done.2 = bf16[128,512]{1,0:T(8,128)(2,1)S(1)} collective-permute-done((bf16[128,512]{1,0:T(8,128)(2,1)S(1)}, bf16[128,512]{1,0:T(8,128)(2,1)S(1)}, u32[]{:S(2)}, u32[]{:S(2)}) %collective-permute-start.2) | collective-permute-done | bytes 131104 | tf_op jit(solution)/shard_map/ppermute | solution.py:73
  31.8 0.8 collective-permute-start.3
  32.5 3.6 %collective-permute-done.8 = bf16[128,512]{1,0:T(8,128)(2,1)S(1)} collective-permute-done((bf16[128,512]{1,0:T(8,128)(2,1)S(1)}, bf16[128,512]{1,0:T(8,128)(2,1)S(1)}, u32[]{:S(2)}, u32[]{:S(2)}) %collective-permute-start.8) | collective-permute-done | bytes 131104 | tf_op jit(solution)/shard_map/ppermute | solution.py:73
  36.2 2.1 %collective-permute-start.9 = (bf16[128,1024]{1,0:T(8,128)(2,1)S(1)}, bf16[128,1024]{1,0:T(8,128)(2,1)S(1)}, u32[]{:S(2)}, u32[]{:S(2)}) collective-permute-start(bf16[128,1024]{1,0:T(8,128)(2,1)S(1)} %pad_maximum_fusion.1), channel_id=1, source_target_pairs={{0,2},{1,5},{2,0},{3,7},{4,6},{5,1},{6,4},{7,3},{8,10},{9,13},{10,... | collective-permute-start | bytes 786440 | tf_op jit(solution)/shard_map/ppermute | solution.py:73
  38.3 0.7 collective-permute-done.3
  39.0 2.1 %collective-permute-start.4 = (bf16[128,1024]{1,0:T(8,128)(2,1)S(1)}, bf16[128,1024]{1,0:T(8,128)(2,1)S(1)}, u32[]{:S(2)}, u32[]{:S(2)}) collective-permute-start(bf16[128,1024]{1,0:T(8,128)(2,1)S(1)} %pad_maximum_fusion), channel_id=1, source_target_pairs={{0,2},{1,5},{2,0},{3,7},{4,6},{5,1},{6,4},{7,3},{8,10},{9,13},{10,... | collective-permute-start | bytes 786440 | tf_op jit(solution)/shard_map/ppermute | solution.py:73
  41.1 1.5 %collective-permute-done.9 = bf16[128,1024]{1,0:T(8,128)(2,1)S(1)} collective-permute-done((bf16[128,1024]{1,0:T(8,128)(2,1)S(1)}, bf16[128,1024]{1,0:T(8,128)(2,1)S(1)}, u32[]{:S(2)}, u32[]{:S(2)}) %collective-permute-start.9) | collective-permute-done | bytes 262176 | tf_op jit(solution)/shard_map/ppermute | solution.py:73
  42.7 0.1 broadcast_select_fusion.1
  42.8 0.7 fusion
  43.5 2.0 %collective-permute-done.4 = bf16[128,1024]{1,0:T(8,128)(2,1)S(1)} collective-permute-done((bf16[128,1024]{1,0:T(8,128)(2,1)S(1)}, bf16[128,1024]{1,0:T(8,128)(2,1)S(1)}, u32[]{:S(2)}, u32[]{:S(2)}) %collective-permute-start.4) | collective-permute-done | bytes 262176 | tf_op jit(solution)/shard_map/ppermute | solution.py:73
  45.5 0.1 broadcast_select_fusion.3
  45.6 0.7 fusion.7.mine_ref
  46.4 1.5 %collective-permute-done.10.other_ref = f32[512,128]{1,0:T(8,128)S(1)} collective-permute-done((f32[512,128]{1,0:T(8,128)S(1)}, f32[512,128]{1,0:T(8,128)S(1)}, u32[]{:S(2)}, u32[]{:S(2)}) %collective-permute-start.10) | collective-permute-done | bytes 262176 | tf_op jit(solution)/shard_map/ppermute | solution.py:28
  47.9 0.5 make_gram.1
  48.4 2.1 %collective-permute-start.11 = (f32[72,128]{1,0:T(8,128)S(1)}, f32[72,128]{1,0:T(8,128)S(1)}, u32[]{:S(2)}, u32[]{:S(2)}) collective-permute-start(f32[72,128]{1,0:T(8,128)S(1)} %make_gram.1), channel_id=1, source_target_pairs={{0,2},{2,0},{4,6},{6,4},{8,10},{10,8},{12,14},{14,12},{1,3},{3,1},... | collective-permute-start | bytes 110600 | tf_op jit(solution)/shard_map/ppermute | solution.py:28
  50.5 1.9 %collective-permute-done.11 = f32[72,128]{1,0:T(8,128)S(1)} collective-permute-done((f32[72,128]{1,0:T(8,128)S(1)}, f32[72,128]{1,0:T(8,128)S(1)}, u32[]{:S(2)}, u32[]{:S(2)}) %collective-permute-start.11) | collective-permute-done | bytes 36896 | tf_op jit(solution)/shard_map/ppermute | solution.py:28
  52.5 1.5 %collective-permute-start.13 = (f32[72,128]{1,0:T(8,128)S(1)}, f32[72,128]{1,0:T(8,128)S(1)}, u32[]{:S(2)}, u32[]{:S(2)}) collective-permute-start(f32[72,128]{1,0:T(8,128)S(1)} %add.93), channel_id=1, source_target_pairs={{0,8},{2,10},{4,12},{6,14},{8,0},{10,2},{12,4},{14,6},{1,9},{3,11}... | collective-permute-start | bytes 110600 | tf_op jit(solution)/shard_map/ppermute | solution.py:28
  54.0 1.5 %collective-permute-start.14 = (f32[72,128]{1,0:T(8,128)S(1)}, f32[72,128]{1,0:T(8,128)S(1)}, u32[]{:S(2)}, u32[]{:S(2)}) collective-permute-start(f32[72,128]{1,0:T(8,128)S(1)} %add.93), channel_id=1, source_target_pairs={{0,12},{2,14},{4,8},{6,10},{8,4},{10,6},{12,0},{14,2},{1,13},{3,15... | collective-permute-start | bytes 110600 | tf_op jit(solution)/shard_map/ppermute | solution.py:28
  55.5 0.5 collective-permute-start.12
  55.9 2.5 %collective-permute-done.13 = f32[72,128]{1,0:T(8,128)S(1)} collective-permute-done((f32[72,128]{1,0:T(8,128)S(1)}, f32[72,128]{1,0:T(8,128)S(1)}, u32[]{:S(2)}, u32[]{:S(2)}) %collective-permute-start.13) | collective-permute-done | bytes 36896 | tf_op jit(solution)/shard_map/ppermute | solution.py:28
  58.5 1.4 %collective-permute-done.14 = f32[72,128]{1,0:T(8,128)S(1)} collective-permute-done((f32[72,128]{1,0:T(8,128)S(1)}, f32[72,128]{1,0:T(8,128)S(1)}, u32[]{:S(2)}, u32[]{:S(2)}) %collective-permute-start.14) | collective-permute-done | bytes 36896 | tf_op jit(solution)/shard_map/ppermute | solution.py:28
  59.8 4.6 %make_basis.1 = (f32[512,128]{1,0:T(8,128)}, f32[128,4096]{1,0:T(8,128)S(1)}) custom-call(f32[72,128]{1,0:T(8,128)S(1)} %add_add_fusion.gram_ref, f32[512,128]{1,0:T(8,128)S(1)} %fusion.7.mine_ref, f32[512,128]{1,0:T(8,128)S(1)} %collective-permute-done.10.other_ref, bf16[512,4096]{1,0:T(8,128)(2,1)} %slab_ref.3), custom_call_target="tpu_custom_call" | custom-call | tf_op jit(solution)/shard_map/make_basis/pallas_call | solution.py:286
  64.5 0.1 fusion.22
  64.7 2.1 %collective-permute-start.19 = (bf16[4,16,2048]{2,1,0:T(8,128)(2,1)S(1)}, bf16[4,16,2048]{2,1,0:T(8,128)(2,1)S(1)}, u32[]{:S(2)}, u32[]{:S(2)}) collective-permute-start(bf16[4,16,2048]{2,1,0:T(8,128)(2,1)S(1)} %fusion.17), channel_id=1, source_target_pairs={{0,2},{2,0},{4,6},{6,4},{8,10},{10,8},{12,14},{14,12},{1,3},{3,1},... | collective-permute-start | bytes 786440 | tf_op jit(solution)/shard_map/ppermute | solution.py:28
  66.8 0.1 collective-permute-start.15
  66.9 6.8 %collective-permute-done.19 = bf16[4,16,2048]{2,1,0:T(8,128)(2,1)S(1)} collective-permute-done((bf16[4,16,2048]{2,1,0:T(8,128)(2,1)S(1)}, bf16[4,16,2048]{2,1,0:T(8,128)(2,1)S(1)}, u32[]{:S(2)}, u32[]{:S(2)}) %collective-permute-start.19) | collective-permute-done | bytes 262176 | tf_op jit(solution)/shard_map/ppermute | solution.py:28
  73.8 1.9 %collective-permute-start.22 = (bf16[1,16,2048]{2,1,0:T(8,128)(2,1)S(1)}, bf16[1,16,2048]{2,1,0:T(8,128)(2,1)S(1)}, u32[]{:S(2)}, u32[]{:S(2)}) collective-permute-start(bf16[1,16,2048]{2,1,0:T(8,128)(2,1)S(1)} %get-tuple-element.16), channel_id=1, source_target_pairs={{0,12},{2,14},{4,8},{6,10},{8,4},{10,6},{12,0},{14,2},{1,13},{3,15... | collective-permute-start | bytes 196616 | tf_op jit(solution)/shard_map/ppermute | solution.py:28
  75.7 0.4 collective-permute-start.21
  76.1 2.2 %collective-permute-start.20 = (bf16[1,16,2048]{2,1,0:T(8,128)(2,1)S(1)}, bf16[1,16,2048]{2,1,0:T(8,128)(2,1)S(1)}, u32[]{:S(2)}, u32[]{:S(2)}) collective-permute-start(bf16[1,16,2048]{2,1,0:T(8,128)(2,1)S(1)} %get-tuple-element.15), channel_id=1, source_target_pairs={{0,4},{2,6},{4,0},{6,2},{8,12},{10,14},{12,8},{14,10},{1,5},{3,7},... | collective-permute-start | bytes 196616 | tf_op jit(solution)/shard_map/ppermute | solution.py:28
  78.4 1.9 %collective-permute-start.18 = (bf16[1,16,2048]{2,1,0:T(8,128)(2,1)S(1)}, bf16[1,16,2048]{2,1,0:T(8,128)(2,1)S(1)}, u32[]{:S(2)}, u32[]{:S(2)}) collective-permute-start(bf16[1,16,2048]{2,1,0:T(8,128)(2,1)S(1)} %get-tuple-element.13), channel_id=1, source_target_pairs={{0,12},{2,14},{4,8},{6,10},{8,4},{10,6},{12,0},{14,2},{1,13},{3,15... | collective-permute-start | bytes 196616 | tf_op jit(solution)/shard_map/ppermute | solution.py:28
  80.2 0.4 collective-permute-done.22
  80.6 2.2 %collective-permute-start.16 = (bf16[1,16,2048]{2,1,0:T(8,128)(2,1)S(1)}, bf16[1,16,2048]{2,1,0:T(8,128)(2,1)S(1)}, u32[]{:S(2)}, u32[]{:S(2)}) collective-permute-start(bf16[1,16,2048]{2,1,0:T(8,128)(2,1)S(1)} %get-tuple-element.12), channel_id=1, source_target_pairs={{0,4},{2,6},{4,0},{6,2},{8,12},{10,14},{12,8},{14,10},{1,5},{3,7},... | collective-permute-start | bytes 196616 | tf_op jit(solution)/shard_map/ppermute | solution.py:28
  82.8 0.3 collective-permute-done.21
  83.1 1.4 %collective-permute-done.18 = bf16[1,16,2048]{2,1,0:T(8,128)(2,1)S(1)} collective-permute-done((bf16[1,16,2048]{2,1,0:T(8,128)(2,1)S(1)}, bf16[1,16,2048]{2,1,0:T(8,128)(2,1)S(1)}, u32[]{:S(2)}, u32[]{:S(2)}) %collective-permute-start.18) | collective-permute-done | bytes 65568 | tf_op jit(solution)/shard_map/ppermute | solution.py:28
  84.5 1.4 %collective-permute-done.17 = bf16[1,16,2048]{2,1,0:T(8,128)(2,1)S(1)} collective-permute-done((bf16[1,16,2048]{2,1,0:T(8,128)(2,1)S(1)}, bf16[1,16,2048]{2,1,0:T(8,128)(2,1)S(1)}, u32[]{:S(2)}, u32[]{:S(2)}) %collective-permute-start.17) | collective-permute-done | bytes 65568 | tf_op jit(solution)/shard_map/ppermute | solution.py:28
  85.9 0.7 pad_maximum_fusion.2
  (35 shorter events, 1.2 us)
Async XLA Ops:
  0.6 0.9 %copy-start = (bf16[512,128]{1,0:T(8,128)(2,1)S(1)}, bf16[512,128]{1,0:T(8,128)(2,1)}, u32[]{:S(2)}) copy-start(bf16[512,128]{1,0:T(8,128)(2,1)} %start_ref.1) | copy-start | bytes 393220
  4.6 7.4 %collective-permute-start.5 = (bf16[128,1024]{1,0:T(8,128)(2,1)S(1)}, bf16[128,1024]{1,0:T(8,128)(2,1)S(1)}, u32[]{:S(2)}, u32[]{:S(2)}) collective-permute-start(bf16[128,1024]{1,0:T(8,128)(2,1)S(1)} %select_convert_fusion), channel_id=1, source_target_pairs={{0,2},{1,5},{2,0},{3,7},{4,6},{5,1},{6,4},{7,3},{8,10},{9,13},{10,... | collective-permute-start | bytes 786440 | tf_op jit(solution)/shard_map/ppermute | solution.py:73
  7.7 7.7 %collective-permute-start = (bf16[128,1024]{1,0:T(8,128)(2,1)S(1)}, bf16[128,1024]{1,0:T(8,128)(2,1)S(1)}, u32[]{:S(2)}, u32[]{:S(2)}) collective-permute-start(bf16[128,1024]{1,0:T(8,128)(2,1)S(1)} %select_convert_fusion.1), channel_id=1, source_target_pairs={{0,2},{1,5},{2,0},{3,7},{4,6},{5,1},{6,4},{7,3},{8,10},{9,13},{10,... | collective-permute-start | bytes 786440 | tf_op jit(solution)/shard_map/ppermute | solution.py:73
  12.1 6.0 %collective-permute-start.6 = (bf16[128,512]{1,0:T(8,128)(2,1)S(1)}, bf16[128,512]{1,0:T(8,128)(2,1)S(1)}, u32[]{:S(2)}, u32[]{:S(2)}) collective-permute-start(bf16[128,512]{1,0:T(8,128)(2,1)S(1)} %select_convert_fusion.2), channel_id=1, source_target_pairs={{0,4},{1,3},{2,6},{3,1},{4,0},{5,7},{6,2},{7,5},{8,12},{9,11},{10,... | collective-permute-start | bytes 393224 | tf_op jit(solution)/shard_map/ppermute | solution.py:73
  15.5 6.6 %collective-permute-start.1 = (bf16[128,512]{1,0:T(8,128)(2,1)S(1)}, bf16[128,512]{1,0:T(8,128)(2,1)S(1)}, u32[]{:S(2)}, u32[]{:S(2)}) collective-permute-start(bf16[128,512]{1,0:T(8,128)(2,1)S(1)} %select_convert_fusion.3), channel_id=1, source_target_pairs={{0,4},{1,3},{2,6},{3,1},{4,0},{5,7},{6,2},{7,5},{8,12},{9,11},{10,... | collective-permute-start | bytes 393224 | tf_op jit(solution)/shard_map/ppermute | solution.py:73
  18.1 12.1 %collective-permute-start.7 = (bf16[128,512]{1,0:T(8,128)(2,1)S(1)}, bf16[128,512]{1,0:T(8,128)(2,1)S(1)}, u32[]{:S(2)}, u32[]{:S(2)}) collective-permute-start(bf16[128,512]{1,0:T(8,128)(2,1)S(1)} %fusion.19), channel_id=1, source_target_pairs={{0,8},{1,9},{2,10},{3,11},{4,12},{5,13},{6,14},{7,15},{8,0},{9,1},... | collective-permute-start | bytes 393224 | tf_op jit(solution)/shard_map/ppermute | solution.py:73
  22.2 9.5 %collective-permute-start.2 = (bf16[128,512]{1,0:T(8,128)(2,1)S(1)}, bf16[128,512]{1,0:T(8,128)(2,1)S(1)}, u32[]{:S(2)}, u32[]{:S(2)}) collective-permute-start(bf16[128,512]{1,0:T(8,128)(2,1)S(1)} %fusion.18), channel_id=1, source_target_pairs={{0,8},{1,9},{2,10},{3,11},{4,12},{5,13},{6,14},{7,15},{8,0},{9,1},... | collective-permute-start | bytes 393224 | tf_op jit(solution)/shard_map/ppermute | solution.py:73
  30.2 12.6 %copy-start.1 = (bf16[512,4096]{1,0:T(8,128)(2,1)S(1)}, bf16[512,4096]{1,0:T(8,128)(2,1)}, u32[]{:S(2)}) copy-start(bf16[512,4096]{1,0:T(8,128)(2,1)} %slab_ref.3) | copy-start | bytes 12582916
  30.3 5.9 %collective-permute-start.8 = (bf16[128,512]{1,0:T(8,128)(2,1)S(1)}, bf16[128,512]{1,0:T(8,128)(2,1)S(1)}, u32[]{:S(2)}, u32[]{:S(2)}) collective-permute-start(bf16[128,512]{1,0:T(8,128)(2,1)S(1)} %multiply_convert_fusion), channel_id=1, source_target_pairs={{0,4},{1,3},{2,6},{3,1},{4,0},{5,7},{6,2},{7,5},{8,12},{9,11},{10,... | collective-permute-start | bytes 393224 | tf_op jit(solution)/shard_map/ppermute | solution.py:73
  31.8 7.2 %collective-permute-start.3 = (bf16[128,512]{1,0:T(8,128)(2,1)S(1)}, bf16[128,512]{1,0:T(8,128)(2,1)S(1)}, u32[]{:S(2)}, u32[]{:S(2)}) collective-permute-start(bf16[128,512]{1,0:T(8,128)(2,1)S(1)} %multiply_convert_fusion.1), channel_id=1, source_target_pairs={{0,4},{1,3},{2,6},{3,1},{4,0},{5,7},{6,2},{7,5},{8,12},{9,11},{10,... | collective-permute-start | bytes 393224 | tf_op jit(solution)/shard_map/ppermute | solution.py:73
  36.2 6.4 %collective-permute-start.9 = (bf16[128,1024]{1,0:T(8,128)(2,1)S(1)}, bf16[128,1024]{1,0:T(8,128)(2,1)S(1)}, u32[]{:S(2)}, u32[]{:S(2)}) collective-permute-start(bf16[128,1024]{1,0:T(8,128)(2,1)S(1)} %pad_maximum_fusion.1), channel_id=1, source_target_pairs={{0,2},{1,5},{2,0},{3,7},{4,6},{5,1},{6,4},{7,3},{8,10},{9,13},{10,... | collective-permute-start | bytes 786440 | tf_op jit(solution)/shard_map/ppermute | solution.py:73
  39.0 6.4 %collective-permute-start.4 = (bf16[128,1024]{1,0:T(8,128)(2,1)S(1)}, bf16[128,1024]{1,0:T(8,128)(2,1)S(1)}, u32[]{:S(2)}, u32[]{:S(2)}) collective-permute-start(bf16[128,1024]{1,0:T(8,128)(2,1)S(1)} %pad_maximum_fusion), channel_id=1, source_target_pairs={{0,2},{1,5},{2,0},{3,7},{4,6},{5,1},{6,4},{7,3},{8,10},{9,13},{10,... | collective-permute-start | bytes 786440 | tf_op jit(solution)/shard_map/ppermute | solution.py:73
  46.3 1.6 %collective-permute-start.10 = (f32[512,128]{1,0:T(8,128)S(1)}, f32[512,128]{1,0:T(8,128)S(1)}, u32[]{:S(2)}, u32[]{:S(2)}) collective-permute-start(f32[512,128]{1,0:T(8,128)S(1)} %fusion.7.mine_ref), channel_id=1, source_target_pairs={{0,1},{1,0},{2,3},{3,2},{4,5},{5,4},{6,7},{7,6},{8,9},{9,8},{10,11... | collective-permute-start | bytes 786440 | tf_op jit(solution)/shard_map/ppermute | solution.py:28
  48.4 4.0 %collective-permute-start.11 = (f32[72,128]{1,0:T(8,128)S(1)}, f32[72,128]{1,0:T(8,128)S(1)}, u32[]{:S(2)}, u32[]{:S(2)}) collective-permute-start(f32[72,128]{1,0:T(8,128)S(1)} %make_gram.1), channel_id=1, source_target_pairs={{0,2},{2,0},{4,6},{6,4},{8,10},{10,8},{12,14},{14,12},{1,3},{3,1},... | collective-permute-start | bytes 110600 | tf_op jit(solution)/shard_map/ppermute | solution.py:28
  52.5 6.0 %collective-permute-start.13 = (f32[72,128]{1,0:T(8,128)S(1)}, f32[72,128]{1,0:T(8,128)S(1)}, u32[]{:S(2)}, u32[]{:S(2)}) collective-permute-start(f32[72,128]{1,0:T(8,128)S(1)} %add.93), channel_id=1, source_target_pairs={{0,8},{2,10},{4,12},{6,14},{8,0},{10,2},{12,4},{14,6},{1,9},{3,11}... | collective-permute-start | bytes 110600 | tf_op jit(solution)/shard_map/ppermute | solution.py:28
  54.0 5.8 %collective-permute-start.14 = (f32[72,128]{1,0:T(8,128)S(1)}, f32[72,128]{1,0:T(8,128)S(1)}, u32[]{:S(2)}, u32[]{:S(2)}) collective-permute-start(f32[72,128]{1,0:T(8,128)S(1)} %add.93), channel_id=1, source_target_pairs={{0,12},{2,14},{4,8},{6,10},{8,4},{10,6},{12,0},{14,2},{1,13},{3,15... | collective-permute-start | bytes 110600 | tf_op jit(solution)/shard_map/ppermute | solution.py:28
  55.5 4.4 %collective-permute-start.12 = (f32[72,128]{1,0:T(8,128)S(1)}, f32[72,128]{1,0:T(8,128)S(1)}, u32[]{:S(2)}, u32[]{:S(2)}) collective-permute-start(f32[72,128]{1,0:T(8,128)S(1)} %add.93), channel_id=1, source_target_pairs={{0,4},{2,6},{4,0},{6,2},{8,12},{10,14},{12,8},{14,10},{1,5},{3,7},... | collective-permute-start | bytes 110600 | tf_op jit(solution)/shard_map/ppermute | solution.py:28
  64.7 9.0 %collective-permute-start.19 = (bf16[4,16,2048]{2,1,0:T(8,128)(2,1)S(1)}, bf16[4,16,2048]{2,1,0:T(8,128)(2,1)S(1)}, u32[]{:S(2)}, u32[]{:S(2)}) collective-permute-start(bf16[4,16,2048]{2,1,0:T(8,128)(2,1)S(1)} %fusion.17), channel_id=1, source_target_pairs={{0,2},{2,0},{4,6},{6,4},{8,10},{10,8},{12,14},{14,12},{1,3},{3,1},... | collective-permute-start | bytes 786440 | tf_op jit(solution)/shard_map/ppermute | solution.py:28
  66.8 11.5 %collective-permute-start.15 = (bf16[4,16,2048]{2,1,0:T(8,128)(2,1)S(1)}, bf16[4,16,2048]{2,1,0:T(8,128)(2,1)S(1)}, u32[]{:S(2)}, u32[]{:S(2)}) collective-permute-start(bf16[4,16,2048]{2,1,0:T(8,128)(2,1)S(1)} %fusion.16), channel_id=1, source_target_pairs={{0,2},{2,0},{4,6},{6,4},{8,10},{10,8},{12,14},{14,12},{1,3},{3,1},... | collective-permute-start | bytes 786440 | tf_op jit(solution)/shard_map/ppermute | solution.py:28
  73.8 6.8 %collective-permute-start.22 = (bf16[1,16,2048]{2,1,0:T(8,128)(2,1)S(1)}, bf16[1,16,2048]{2,1,0:T(8,128)(2,1)S(1)}, u32[]{:S(2)}, u32[]{:S(2)}) collective-permute-start(bf16[1,16,2048]{2,1,0:T(8,128)(2,1)S(1)} %get-tuple-element.16), channel_id=1, source_target_pairs={{0,12},{2,14},{4,8},{6,10},{8,4},{10,6},{12,0},{14,2},{1,13},{3,15... | collective-permute-start | bytes 196616 | tf_op jit(solution)/shard_map/ppermute | solution.py:28
  75.7 7.4 %collective-permute-start.21 = (bf16[1,16,2048]{2,1,0:T(8,128)(2,1)S(1)}, bf16[1,16,2048]{2,1,0:T(8,128)(2,1)S(1)}, u32[]{:S(2)}, u32[]{:S(2)}) collective-permute-start(bf16[1,16,2048]{2,1,0:T(8,128)(2,1)S(1)} %get-tuple-element.17), channel_id=1, source_target_pairs={{0,8},{2,10},{4,12},{6,14},{8,0},{10,2},{12,4},{14,6},{1,9},{3,11}... | collective-permute-start | bytes 196616 | tf_op jit(solution)/shard_map/ppermute | solution.py:28
  76.1 7.0 %collective-permute-start.20 = (bf16[1,16,2048]{2,1,0:T(8,128)(2,1)S(1)}, bf16[1,16,2048]{2,1,0:T(8,128)(2,1)S(1)}, u32[]{:S(2)}, u32[]{:S(2)}) collective-permute-start(bf16[1,16,2048]{2,1,0:T(8,128)(2,1)S(1)} %get-tuple-element.15), channel_id=1, source_target_pairs={{0,4},{2,6},{4,0},{6,2},{8,12},{10,14},{12,8},{14,10},{1,5},{3,7},... | collective-permute-start | bytes 196616 | tf_op jit(solution)/shard_map/ppermute | solution.py:28
  78.4 6.1 %collective-permute-start.18 = (bf16[1,16,2048]{2,1,0:T(8,128)(2,1)S(1)}, bf16[1,16,2048]{2,1,0:T(8,128)(2,1)S(1)}, u32[]{:S(2)}, u32[]{:S(2)}) collective-permute-start(bf16[1,16,2048]{2,1,0:T(8,128)(2,1)S(1)} %get-tuple-element.13), channel_id=1, source_target_pairs={{0,12},{2,14},{4,8},{6,10},{8,4},{10,6},{12,0},{14,2},{1,13},{3,15... | collective-permute-start | bytes 196616 | tf_op jit(solution)/shard_map/ppermute | solution.py:28
  80.2 5.7 %collective-permute-start.17 = (bf16[1,16,2048]{2,1,0:T(8,128)(2,1)S(1)}, bf16[1,16,2048]{2,1,0:T(8,128)(2,1)S(1)}, u32[]{:S(2)}, u32[]{:S(2)}) collective-permute-start(bf16[1,16,2048]{2,1,0:T(8,128)(2,1)S(1)} %get-tuple-element.14), channel_id=1, source_target_pairs={{0,8},{2,10},{4,12},{6,14},{8,0},{10,2},{12,4},{14,6},{1,9},{3,11}... | collective-permute-start | bytes 196616 | tf_op jit(solution)/shard_map/ppermute | solution.py:28
  80.6 5.3 %collective-permute-start.16 = (bf16[1,16,2048]{2,1,0:T(8,128)(2,1)S(1)}, bf16[1,16,2048]{2,1,0:T(8,128)(2,1)S(1)}, u32[]{:S(2)}, u32[]{:S(2)}) collective-permute-start(bf16[1,16,2048]{2,1,0:T(8,128)(2,1)S(1)} %get-tuple-element.12), channel_id=1, source_target_pairs={{0,4},{2,6},{4,0},{6,2},{8,12},{10,14},{12,8},{14,10},{1,5},{3,7},... | collective-permute-start | bytes 196616 | tf_op jit(solution)/shard_map/ppermute | solution.py:28

commit v12 on v10

--- a/solution.py
+++ b/solution.py
@@ -28,12 +28,26 @@
     return lax.ppermute(value, axis, [(i, i ^ distance) for i in range(size)])
 
 
-def exchange_sum(value, axis):
-    for stride, radix in levels_of(lax.axis_size(axis)):
-        terms = [value] + [swap(value, axis, t * stride) for t in range(1, radix)]
+def row_sum(value):
+    rows, cores = lax.axis_size("row"), lax.axis_size("col")
+    assert cores == 2
+    first = lax.axis_index("col") == 0
+    stride = 1
+    while stride < rows:
+        radix = min(8, rows // stride)
+        terms = []
+        for t in range(radix // 2):
+            pairs = []
+            for row in range(rows):
+                for core, digit in ((0, t), (1, t + radix // 2)):
+                    if digit:
+                        pairs.append((row * cores + core, (row ^ digit * stride) * cores + core))
+            terms.append(lax.ppermute(value, ("row", "col"), pairs))
+        terms[0] = jnp.where(first, value, terms[0])
         while len(terms) > 1:
             terms = [terms[i] + terms[i + 1] for i in range(0, len(terms), 2)]
-        value = terms[0]
+        value = terms[0] + swap(terms[0], "col", 1)
+        stride *= radix
     return value
 
 
@@ -317,7 +331,7 @@
             preferred_element_type=jnp.float32,
         )
     other_sketch = swap(partial_sketch, "col", 1)
-    gram = exchange_sum(make_gram(partial_sketch, other_sketch, total_cols), "row")
+    gram = row_sum(make_gram(partial_sketch, other_sketch, total_cols))
     basis, local_proj = make_basis(
         gram, partial_sketch, other_sketch, activations, total_cols, root_rows
     )

time: 83.7 us -> 85.5 us (1.022)
  starting transfers between devices: 41.9 us -> 45.4 us
  waiting for transfers between devices: 27.8 us -> 26.1 us
    ppermute x0 -> x4, starting transfers between devices: none -> 4.21 us  [row_sum(): terms.append(lax.ppermute(value, ('row', 'col'), pairs))]
    ppermute x33 -> x30, waiting for transfers between devices: 27.8 us -> 23.9 us  [swap(): return lax.ppermute(value, axis, [(i, i ^ distance) for i in range(size)])]
    ppermute x0 -> x4, waiting for transfers between devices: none -> 2.25 us  [row_sum(): terms.append(lax.ppermute(value, ('row', 'col'), pairs))]
    ppermute x33 -> x30, starting transfers between devices: 41.9 us -> 41.2 us  [swap(): return lax.ppermute(value, axis, [(i, i ^ distance) for i in range(size)])]
  transfers between devices with their start and end apart: 33 -> 34, of which waited for: 19 -> 18; matrix products, arithmetic and copies ran while one was open for 3% -> 3% of each run, Pallas kernels for 0% -> 0%
where the time goes in v12:
time: 85.5 us; the launch traced here: 85.4 us
  starting transfers between devices  45.4 us (53%)
  waiting for transfers between devices  26.1 us (31%)
  Pallas kernels  8.12 us (9%)
  other arithmetic  1.8 us (2%)
  matrix products  1.74 us (2%)
  local copies, waits for them, and re-layouts  1.17 us (1%)
  between operations  0.99 us (1%)
    ppermute x30, starting transfers between devices, swap(): return lax.ppermute(value, axis, [(i, i ^ distance) for i in range(size)])  41.2 us
    ppermute x30, waiting for transfers between devices, swap(): return lax.ppermute(value, axis, [(i, i ^ distance) for i in range(size)])  23.9 us
    pallas_call x1, Pallas kernels, make_basis(): pl.pallas_call(functools.partial(basis_kernel, total_cols, root_rows), ou...  4.63 us
    ppermute x4, starting transfers between devices, row_sum(): terms.append(lax.ppermute(value, ('row', 'col'), pairs))  4.21 us
    pallas_call x1, Pallas kernels, first_product(): pl.pallas_call(sketch_kernel, out_shape=[jax.ShapeDtypeStruct((width, col...  3 us
    ppermute x4, waiting for transfers between devices, row_sum(): terms.append(lax.ppermute(value, ('row', 'col'), pairs))  2.25 us
    dot_general x4, matrix products, per_device(): lax.dot_general(activations[:, span], shared, (((1,), (1,)), ((), ())), p...  1.74 us
  transfers between devices with their start and end apart: 34, of which 18 were waited for; matrix products, arithmetic and copies ran while one was open for 3% of the time, Pallas kernels for 0%

profile of v12, /device:TPU:0, one launch (start us, length us, event | category | flops | bytes accessed | tf_op | source)
XLA Modules:
  0.0 85.4 jit_solution(7510247445467984149)
XLA Ops:
  0.7 0.9 %copy-done = bf16[512,128]{1,0:T(8,128)(2,1)S(1)} copy-done((bf16[512,128]{1,0:T(8,128)(2,1)S(1)}, bf16[512,128]{1,0:T(8,128)(2,1)}, u32[]{:S(2)}) %copy-start) | copy-done | bytes 131096
  1.6 3.0 %first_product.1 = (f32[128,1024]{1,0:T(8,128)S(1)}, f32[128,1024]{1,0:T(8,128)S(1)}, f32[128,1024]{1,0:T(8,128)S(1)}, f32[128,1024]{1,0:T(8,128)S(1)}) custom-call(bf16[512,128]{1,0:T(8,128)(2,1)S(1)} %copy-done, bf16[512,4096]{1,0:T(8,128)(2,1)} %slab_ref.3), custom_call_target="tpu_custom_call" | custom-call | flops 536870912 | bytes 4194304 | tf_op jit(solution)/shard_map/first_product/pallas_call | solution.py:132
  4.6 3.1 %collective-permute-start.15 = (bf16[128,512]{1,0:T(8,128)(2,1)S(1)}, bf16[128,512]{1,0:T(8,128)(2,1)S(1)}, u32[]{:S(2)}, u32[]{:S(2)}) collective-permute-start(bf16[128,512]{1,0:T(8,128)(2,1)S(1)} %select_convert_fusion), channel_id=1, source_target_pairs={{0,4},{2,6},{4,0},{6,2},{8,12},{10,14},{12,8},{14,10},{1,5},{3,7},... | collective-permute-start | bytes 393224 | tf_op jit(solution)/shard_map/ppermute | solution.py:28
  7.7 1.6 %collective-permute-start.10 = (bf16[128,512]{1,0:T(8,128)(2,1)S(1)}, bf16[128,512]{1,0:T(8,128)(2,1)S(1)}, u32[]{:S(2)}, u32[]{:S(2)}) collective-permute-start(bf16[128,512]{1,0:T(8,128)(2,1)S(1)} %select_convert_fusion.1), channel_id=1, source_target_pairs={{0,2},{2,0},{4,6},{6,4},{8,10},{10,8},{12,14},{14,12},{1,3},{3,1},... | collective-permute-start | bytes 393224 | tf_op jit(solution)/shard_map/ppermute | solution.py:28
  9.3 0.5 collective-permute-start.5
  10.0 1.6 %collective-permute-done.15 = bf16[128,512]{1,0:T(8,128)(2,1)S(1)} collective-permute-done((bf16[128,512]{1,0:T(8,128)(2,1)S(1)}, bf16[128,512]{1,0:T(8,128)(2,1)S(1)}, u32[]{:S(2)}, u32[]{:S(2)}) %collective-permute-start.15) | collective-permute-done | bytes 131104 | tf_op jit(solution)/shard_map/ppermute | solution.py:28
  11.7 2.4 %collective-permute-start.16 = (bf16[128,256]{1,0:T(8,128)(2,1)S(1)}, bf16[128,256]{1,0:T(8,128)(2,1)S(1)}, u32[]{:S(2)}, u32[]{:S(2)}) collective-permute-start(bf16[128,256]{1,0:T(8,128)(2,1)S(1)} %select_convert_fusion.4), channel_id=1, source_target_pairs={{0,2},{2,0},{4,6},{6,4},{8,10},{10,8},{12,14},{14,12},{1,3},{3,1},... | collective-permute-start | bytes 196616 | tf_op jit(solution)/shard_map/ppermute | solution.py:28
  14.1 1.7 %collective-permute-start.11 = (bf16[128,256]{1,0:T(8,128)(2,1)S(1)}, bf16[128,256]{1,0:T(8,128)(2,1)S(1)}, u32[]{:S(2)}, u32[]{:S(2)}) collective-permute-start(bf16[128,256]{1,0:T(8,128)(2,1)S(1)} %select_convert_fusion.5), channel_id=1, source_target_pairs={{0,4},{2,6},{4,0},{6,2},{8,12},{10,14},{12,8},{14,10},{1,5},{3,7},... | collective-permute-start | bytes 196616 | tf_op jit(solution)/shard_map/ppermute | solution.py:28
  16.0 0.6 collective-permute-start.6
  16.7 1.5 %collective-permute-start.1 = (bf16[128,256]{1,0:T(8,128)(2,1)S(1)}, bf16[128,256]{1,0:T(8,128)(2,1)S(1)}, u32[]{:S(2)}, u32[]{:S(2)}) collective-permute-start(bf16[128,256]{1,0:T(8,128)(2,1)S(1)} %select_convert_fusion.7), channel_id=1, source_target_pairs={{0,4},{2,6},{4,0},{6,2},{8,12},{10,14},{12,8},{14,10},{1,5},{3,7},... | collective-permute-start | bytes 196616 | tf_op jit(solution)/shard_map/ppermute | solution.py:28
  18.2 2.6 %collective-permute-start.17 = (bf16[128,256]{1,0:T(8,128)(2,1)S(1)}, bf16[128,256]{1,0:T(8,128)(2,1)S(1)}, u32[]{:S(2)}, u32[]{:S(2)}) collective-permute-start(bf16[128,256]{1,0:T(8,128)(2,1)S(1)} %fusion.27), channel_id=1, source_target_pairs={{0,8},{2,10},{4,12},{6,14},{8,0},{10,2},{12,4},{14,6},{1,9},{3,11}... | collective-permute-start | bytes 196616 | tf_op jit(solution)/shard_map/ppermute | solution.py:28
  20.9 0.9 %collective-permute-start.12 = (bf16[128,256]{1,0:T(8,128)(2,1)S(1)}, bf16[128,256]{1,0:T(8,128)(2,1)S(1)}, u32[]{:S(2)}, u32[]{:S(2)}) collective-permute-start(bf16[128,256]{1,0:T(8,128)(2,1)S(1)} %fusion.26), channel_id=1, source_target_pairs={{0,8},{2,10},{4,12},{6,14},{8,0},{10,2},{12,4},{14,6},{1,9},{3,11}... | collective-permute-start | bytes 196616 | tf_op jit(solution)/shard_map/ppermute | solution.py:28
  21.8 2.2 %collective-permute-start.7 = (bf16[128,256]{1,0:T(8,128)(2,1)S(1)}, bf16[128,256]{1,0:T(8,128)(2,1)S(1)}, u32[]{:S(2)}, u32[]{:S(2)}) collective-permute-start(bf16[128,256]{1,0:T(8,128)(2,1)S(1)} %fusion.25), channel_id=1, source_target_pairs={{0,8},{2,10},{4,12},{6,14},{8,0},{10,2},{12,4},{14,6},{1,9},{3,11}... | collective-permute-start | bytes 196616 | tf_op jit(solution)/shard_map/ppermute | solution.py:28
  24.0 0.9 %collective-permute-start.2 = (bf16[128,256]{1,0:T(8,128)(2,1)S(1)}, bf16[128,256]{1,0:T(8,128)(2,1)S(1)}, u32[]{:S(2)}, u32[]{:S(2)}) collective-permute-start(bf16[128,256]{1,0:T(8,128)(2,1)S(1)} %fusion.24), channel_id=1, source_target_pairs={{0,8},{2,10},{4,12},{6,14},{8,0},{10,2},{12,4},{14,6},{1,9},{3,11}... | collective-permute-start | bytes 196616 | tf_op jit(solution)/shard_map/ppermute | solution.py:28
  24.9 2.2 %collective-permute-done.17 = bf16[128,256]{1,0:T(8,128)(2,1)S(1)} collective-permute-done((bf16[128,256]{1,0:T(8,128)(2,1)S(1)}, bf16[128,256]{1,0:T(8,128)(2,1)S(1)}, u32[]{:S(2)}, u32[]{:S(2)}) %collective-permute-start.17) | collective-permute-done | bytes 65568 | tf_op jit(solution)/shard_map/ppermute | solution.py:28
  27.1 1.8 %collective-permute-start.18 = (bf16[128,256]{1,0:T(8,128)(2,1)S(1)}, bf16[128,256]{1,0:T(8,128)(2,1)S(1)}, u32[]{:S(2)}, u32[]{:S(2)}) collective-permute-start(bf16[128,256]{1,0:T(8,128)(2,1)S(1)} %multiply_convert_fusion), channel_id=1, source_target_pairs={{0,2},{2,0},{4,6},{6,4},{8,10},{10,8},{12,14},{14,12},{1,3},{3,1},... | collective-permute-start | bytes 196616 | tf_op jit(solution)/shard_map/ppermute | solution.py:28
  28.9 1.1 %collective-permute-done.12 = bf16[128,256]{1,0:T(8,128)(2,1)S(1)} collective-permute-done((bf16[128,256]{1,0:T(8,128)(2,1)S(1)}, bf16[128,256]{1,0:T(8,128)(2,1)S(1)}, u32[]{:S(2)}, u32[]{:S(2)}) %collective-permute-start.12) | collective-permute-done | bytes 65568 | tf_op jit(solution)/shard_map/ppermute | solution.py:28
  30.1 1.0 %collective-permute-done.7 = bf16[128,256]{1,0:T(8,128)(2,1)S(1)} collective-permute-done((bf16[128,256]{1,0:T(8,128)(2,1)S(1)}, bf16[128,256]{1,0:T(8,128)(2,1)S(1)}, u32[]{:S(2)}, u32[]{:S(2)}) %collective-permute-start.7) | collective-permute-done | bytes 65568 | tf_op jit(solution)/shard_map/ppermute | solution.py:28
  31.1 1.2 %collective-permute-start.8 = (bf16[128,256]{1,0:T(8,128)(2,1)S(1)}, bf16[128,256]{1,0:T(8,128)(2,1)S(1)}, u32[]{:S(2)}, u32[]{:S(2)}) collective-permute-start(bf16[128,256]{1,0:T(8,128)(2,1)S(1)} %multiply_convert_fusion.2), channel_id=1, source_target_pairs={{0,2},{2,0},{4,6},{6,4},{8,10},{10,8},{12,14},{14,12},{1,3},{3,1},... | collective-permute-start | bytes 196616 | tf_op jit(solution)/shard_map/ppermute | solution.py:28
  32.3 1.1 %collective-permute-start.3 = (bf16[128,256]{1,0:T(8,128)(2,1)S(1)}, bf16[128,256]{1,0:T(8,128)(2,1)S(1)}, u32[]{:S(2)}, u32[]{:S(2)}) collective-permute-start(bf16[128,256]{1,0:T(8,128)(2,1)S(1)} %multiply_convert_fusion.3), channel_id=1, source_target_pairs={{0,4},{2,6},{4,0},{6,2},{8,12},{10,14},{12,8},{14,10},{1,5},{3,7},... | collective-permute-start | bytes 196616 | tf_op jit(solution)/shard_map/ppermute | solution.py:28
  33.5 1.0 %collective-permute-start.19 = (bf16[128,512]{1,0:T(8,128)(2,1)S(1)}, bf16[128,512]{1,0:T(8,128)(2,1)S(1)}, u32[]{:S(2)}, u32[]{:S(2)}) collective-permute-start(bf16[128,512]{1,0:T(8,128)(2,1)S(1)} %pad_maximum_fusion.4), channel_id=1, source_target_pairs={{0,4},{2,6},{4,0},{6,2},{8,12},{10,14},{12,8},{14,10},{1,5},{3,7},... | collective-permute-start | bytes 393224 | tf_op jit(solution)/shard_map/ppermute | solution.py:28
  35.1 1.2 %collective-permute-start.14 = (bf16[128,512]{1,0:T(8,128)(2,1)S(1)}, bf16[128,512]{1,0:T(8,128)(2,1)S(1)}, u32[]{:S(2)}, u32[]{:S(2)}) collective-permute-start(bf16[128,512]{1,0:T(8,128)(2,1)S(1)} %pad_maximum_fusion.3), channel_id=1, source_target_pairs={{0,2},{2,0},{4,6},{6,4},{8,10},{10,8},{12,14},{14,12},{1,3},{3,1},... | collective-permute-start | bytes 393224 | tf_op jit(solution)/shard_map/ppermute | solution.py:28
  36.3 0.9 %collective-permute-start.9 = (bf16[128,512]{1,0:T(8,128)(2,1)S(1)}, bf16[128,512]{1,0:T(8,128)(2,1)S(1)}, u32[]{:S(2)}, u32[]{:S(2)}) collective-permute-start(bf16[128,512]{1,0:T(8,128)(2,1)S(1)} %pad_maximum_fusion.2), channel_id=1, source_target_pairs={{0,4},{2,6},{4,0},{6,2},{8,12},{10,14},{12,8},{14,10},{1,5},{3,7},... | collective-permute-start | bytes 393224 | tf_op jit(solution)/shard_map/ppermute | solution.py:28
  37.5 1.1 %collective-permute-start.4 = (bf16[128,512]{1,0:T(8,128)(2,1)S(1)}, bf16[128,512]{1,0:T(8,128)(2,1)S(1)}, u32[]{:S(2)}, u32[]{:S(2)}) collective-permute-start(bf16[128,512]{1,0:T(8,128)(2,1)S(1)} %pad_maximum_fusion.1), channel_id=1, source_target_pairs={{0,2},{2,0},{4,6},{6,4},{8,10},{10,8},{12,14},{14,12},{1,3},{3,1},... | collective-permute-start | bytes 393224 | tf_op jit(solution)/shard_map/ppermute | solution.py:28
  38.5 1.4 %collective-permute-done.19 = bf16[128,512]{1,0:T(8,128)(2,1)S(1)} collective-permute-done((bf16[128,512]{1,0:T(8,128)(2,1)S(1)}, bf16[128,512]{1,0:T(8,128)(2,1)S(1)}, u32[]{:S(2)}, u32[]{:S(2)}) %collective-permute-start.19) | collective-permute-done | bytes 131104 | tf_op jit(solution)/shard_map/ppermute | solution.py:28
  41.9 0.6 collective-permute-done.4
  43.1 1.5 %collective-permute-done.20.other_ref = f32[512,128]{1,0:T(8,128)S(1)} collective-permute-done((f32[512,128]{1,0:T(8,128)S(1)}, f32[512,128]{1,0:T(8,128)S(1)}, u32[]{:S(2)}, u32[]{:S(2)}) %collective-permute-start.20) | collective-permute-done | bytes 262176 | tf_op jit(solution)/shard_map/ppermute | solution.py:28
  45.1 1.1 %collective-permute-start.23 = (f32[72,128]{1,0:T(8,128)S(1)}, f32[72,128]{1,0:T(8,128)S(1)}, u32[]{:S(2)}, u32[]{:S(2)}) collective-permute-start(f32[72,128]{1,0:T(8,128)S(1)} %make_gram.1), channel_id=1, source_target_pairs={{0,4},{1,13},{2,6},{3,15},{4,0},{5,9},{6,2},{7,11},{8,12},{9,5},{1... | collective-permute-start | bytes 110600 | tf_op jit(solution)/shard_map/ppermute | solution.py:45
  46.2 1.4 %collective-permute-start.24 = (f32[72,128]{1,0:T(8,128)S(1)}, f32[72,128]{1,0:T(8,128)S(1)}, u32[]{:S(2)}, u32[]{:S(2)}) collective-permute-start(f32[72,128]{1,0:T(8,128)S(1)} %make_gram.1), channel_id=1, source_target_pairs={{0,6},{1,15},{2,4},{3,13},{4,2},{5,11},{6,0},{7,9},{8,14},{9,7},{1... | collective-permute-start | bytes 110600 | tf_op jit(solution)/shard_map/ppermute | solution.py:45
  47.6 1.0 %collective-permute-start.22 = (f32[72,128]{1,0:T(8,128)S(1)}, f32[72,128]{1,0:T(8,128)S(1)}, u32[]{:S(2)}, u32[]{:S(2)}) collective-permute-start(f32[72,128]{1,0:T(8,128)S(1)} %make_gram.1), channel_id=1, source_target_pairs={{0,2},{1,11},{2,0},{3,9},{4,6},{5,15},{6,4},{7,13},{8,10},{9,3},{1... | collective-permute-start | bytes 110600 | tf_op jit(solution)/shard_map/ppermute | solution.py:45
  48.6 0.7 collective-permute-start.21
  49.3 1.8 %collective-permute-done.24 = f32[72,128]{1,0:T(8,128)S(1)} collective-permute-done((f32[72,128]{1,0:T(8,128)S(1)}, f32[72,128]{1,0:T(8,128)S(1)}, u32[]{:S(2)}, u32[]{:S(2)}) %collective-permute-start.24) | collective-permute-done | bytes 36896 | tf_op jit(solution)/shard_map/ppermute | solution.py:45
  51.6 3.6 %collective-permute-start.25 = (f32[72,128]{1,0:T(8,128)S(1)}, f32[72,128]{1,0:T(8,128)S(1)}, u32[]{:S(2)}, u32[]{:S(2)}) collective-permute-start(f32[72,128]{1,0:T(8,128)S(1)} %add_add_fusion), channel_id=1, source_target_pairs={{0,1},{1,0},{2,3},{3,2},{4,5},{5,4},{6,7},{7,6},{8,9},{9,8},{10,11... | collective-permute-start | bytes 110600 | tf_op jit(solution)/shard_map/ppermute | solution.py:28
  55.1 0.9 %collective-permute-done.25 = f32[72,128]{1,0:T(8,128)S(1)} collective-permute-done((f32[72,128]{1,0:T(8,128)S(1)}, f32[72,128]{1,0:T(8,128)S(1)}, u32[]{:S(2)}, u32[]{:S(2)}) %collective-permute-start.25) | collective-permute-done | bytes 36896 | tf_op jit(solution)/shard_map/ppermute | solution.py:28
  56.0 4.6 %make_basis.1 = (f32[512,128]{1,0:T(8,128)}, f32[128,4096]{1,0:T(8,128)S(1)}) custom-call(f32[72,128]{1,0:T(8,128)S(1)} %add.130.gram_ref, f32[512,128]{1,0:T(8,128)S(1)} %fusion.2.mine_ref, f32[512,128]{1,0:T(8,128)S(1)} %collective-permute-done.20.other_ref, bf16[512,4096]{1,0:T(8,128)(2,1)} %slab_ref.3), custom_call_target="tpu_custom_call" | custom-call | tf_op jit(solution)/shard_map/make_basis/pallas_call | solution.py:289
  60.8 1.1 %collective-permute-start.30 = (bf16[4,16,2048]{2,1,0:T(8,128)(2,1)S(1)}, bf16[4,16,2048]{2,1,0:T(8,128)(2,1)S(1)}, u32[]{:S(2)}, u32[]{:S(2)}) collective-permute-start(bf16[4,16,2048]{2,1,0:T(8,128)(2,1)S(1)} %fusion.11), channel_id=1, source_target_pairs={{0,2},{2,0},{4,6},{6,4},{8,10},{10,8},{12,14},{14,12},{1,3},{3,1},... | collective-permute-start | bytes 786440 | tf_op jit(solution)/shard_map/ppermute | solution.py:28
  61.9 1.1 %collective-permute-start.26 = (bf16[4,16,2048]{2,1,0:T(8,128)(2,1)S(1)}, bf16[4,16,2048]{2,1,0:T(8,128)(2,1)S(1)}, u32[]{:S(2)}, u32[]{:S(2)}) collective-permute-start(bf16[4,16,2048]{2,1,0:T(8,128)(2,1)S(1)} %fusion.10), channel_id=1, source_target_pairs={{0,2},{2,0},{4,6},{6,4},{8,10},{10,8},{12,14},{14,12},{1,3},{3,1},... | collective-permute-start | bytes 786440 | tf_op jit(solution)/shard_map/ppermute | solution.py:28
  63.0 7.0 %collective-permute-done.30 = bf16[4,16,2048]{2,1,0:T(8,128)(2,1)S(1)} collective-permute-done((bf16[4,16,2048]{2,1,0:T(8,128)(2,1)S(1)}, bf16[4,16,2048]{2,1,0:T(8,128)(2,1)S(1)}, u32[]{:S(2)}, u32[]{:S(2)}) %collective-permute-start.30) | collective-permute-done | bytes 262176 | tf_op jit(solution)/shard_map/ppermute | solution.py:28
  70.1 1.9 %collective-permute-start.33 = (bf16[1,16,2048]{2,1,0:T(8,128)(2,1)S(1)}, bf16[1,16,2048]{2,1,0:T(8,128)(2,1)S(1)}, u32[]{:S(2)}, u32[]{:S(2)}) collective-permute-start(bf16[1,16,2048]{2,1,0:T(8,128)(2,1)S(1)} %get-tuple-element.20), channel_id=1, source_target_pairs={{0,12},{2,14},{4,8},{6,10},{8,4},{10,6},{12,0},{14,2},{1,13},{3,15... | collective-permute-start | bytes 196616 | tf_op jit(solution)/shard_map/ppermute | solution.py:28
  72.1 1.7 %collective-permute-start.32 = (bf16[1,16,2048]{2,1,0:T(8,128)(2,1)S(1)}, bf16[1,16,2048]{2,1,0:T(8,128)(2,1)S(1)}, u32[]{:S(2)}, u32[]{:S(2)}) collective-permute-start(bf16[1,16,2048]{2,1,0:T(8,128)(2,1)S(1)} %get-tuple-element.21), channel_id=1, source_target_pairs={{0,8},{2,10},{4,12},{6,14},{8,0},{10,2},{12,4},{14,6},{1,9},{3,11}... | collective-permute-start | bytes 196616 | tf_op jit(solution)/shard_map/ppermute | solution.py:28
  73.8 0.8 collective-permute-start.31
  74.6 0.5 collective-permute-done.26
  75.2 1.9 %collective-permute-start.29 = (bf16[1,16,2048]{2,1,0:T(8,128)(2,1)S(1)}, bf16[1,16,2048]{2,1,0:T(8,128)(2,1)S(1)}, u32[]{:S(2)}, u32[]{:S(2)}) collective-permute-start(bf16[1,16,2048]{2,1,0:T(8,128)(2,1)S(1)} %get-tuple-element.17), channel_id=1, source_target_pairs={{0,12},{2,14},{4,8},{6,10},{8,4},{10,6},{12,0},{14,2},{1,13},{3,15... | collective-permute-start | bytes 196616 | tf_op jit(solution)/shard_map/ppermute | solution.py:28
  77.1 1.7 %collective-permute-start.28 = (bf16[1,16,2048]{2,1,0:T(8,128)(2,1)S(1)}, bf16[1,16,2048]{2,1,0:T(8,128)(2,1)S(1)}, u32[]{:S(2)}, u32[]{:S(2)}) collective-permute-start(bf16[1,16,2048]{2,1,0:T(8,128)(2,1)S(1)} %get-tuple-element.18), channel_id=1, source_target_pairs={{0,8},{2,10},{4,12},{6,14},{8,0},{10,2},{12,4},{14,6},{1,9},{3,11}... | collective-permute-start | bytes 196616 | tf_op jit(solution)/shard_map/ppermute | solution.py:28
  78.9 0.8 collective-permute-start.27
  79.7 2.4 %collective-permute-done.29 = bf16[1,16,2048]{2,1,0:T(8,128)(2,1)S(1)} collective-permute-done((bf16[1,16,2048]{2,1,0:T(8,128)(2,1)S(1)}, bf16[1,16,2048]{2,1,0:T(8,128)(2,1)S(1)}, u32[]{:S(2)}, u32[]{:S(2)}) %collective-permute-start.29) | collective-permute-done | bytes 65568 | tf_op jit(solution)/shard_map/ppermute | solution.py:28
  82.1 2.5 %collective-permute-done.28 = bf16[1,16,2048]{2,1,0:T(8,128)(2,1)S(1)} collective-permute-done((bf16[1,16,2048]{2,1,0:T(8,128)(2,1)S(1)}, bf16[1,16,2048]{2,1,0:T(8,128)(2,1)S(1)}, u32[]{:S(2)}, u32[]{:S(2)}) %collective-permute-start.28) | collective-permute-done | bytes 65568 | tf_op jit(solution)/shard_map/ppermute | solution.py:28
  84.6 0.7 pad_maximum_fusion
  (75 shorter events, 5.5 us)
Async XLA Ops:
  0.6 0.9 %copy-start = (bf16[512,128]{1,0:T(8,128)(2,1)S(1)}, bf16[512,128]{1,0:T(8,128)(2,1)}, u32[]{:S(2)}) copy-start(bf16[512,128]{1,0:T(8,128)(2,1)} %start_ref.1) | copy-start | bytes 393220
  4.6 7.0 %collective-permute-start.15 = (bf16[128,512]{1,0:T(8,128)(2,1)S(1)}, bf16[128,512]{1,0:T(8,128)(2,1)S(1)}, u32[]{:S(2)}, u32[]{:S(2)}) collective-permute-start(bf16[128,512]{1,0:T(8,128)(2,1)S(1)} %select_convert_fusion), channel_id=1, source_target_pairs={{0,4},{2,6},{4,0},{6,2},{8,12},{10,14},{12,8},{14,10},{1,5},{3,7},... | collective-permute-start | bytes 393224 | tf_op jit(solution)/shard_map/ppermute | solution.py:28
  7.7 6.3 %collective-permute-start.10 = (bf16[128,512]{1,0:T(8,128)(2,1)S(1)}, bf16[128,512]{1,0:T(8,128)(2,1)S(1)}, u32[]{:S(2)}, u32[]{:S(2)}) collective-permute-start(bf16[128,512]{1,0:T(8,128)(2,1)S(1)} %select_convert_fusion.1), channel_id=1, source_target_pairs={{0,2},{2,0},{4,6},{6,4},{8,10},{10,8},{12,14},{14,12},{1,3},{3,1},... | collective-permute-start | bytes 393224 | tf_op jit(solution)/shard_map/ppermute | solution.py:28
  9.3 6.6 %collective-permute-start.5 = (bf16[128,512]{1,0:T(8,128)(2,1)S(1)}, bf16[128,512]{1,0:T(8,128)(2,1)S(1)}, u32[]{:S(2)}, u32[]{:S(2)}) collective-permute-start(bf16[128,512]{1,0:T(8,128)(2,1)S(1)} %select_convert_fusion.2), channel_id=1, source_target_pairs={{0,4},{2,6},{4,0},{6,2},{8,12},{10,14},{12,8},{14,10},{1,5},{3,7},... | collective-permute-start | bytes 393224 | tf_op jit(solution)/shard_map/ppermute | solution.py:28
  9.8 6.7 %collective-permute-start = (bf16[128,512]{1,0:T(8,128)(2,1)S(1)}, bf16[128,512]{1,0:T(8,128)(2,1)S(1)}, u32[]{:S(2)}, u32[]{:S(2)}) collective-permute-start(bf16[128,512]{1,0:T(8,128)(2,1)S(1)} %select_convert_fusion.3), channel_id=1, source_target_pairs={{0,2},{2,0},{4,6},{6,4},{8,10},{10,8},{12,14},{14,12},{1,3},{3,1},... | collective-permute-start | bytes 393224 | tf_op jit(solution)/shard_map/ppermute | solution.py:28
  11.7 6.5 %collective-permute-start.16 = (bf16[128,256]{1,0:T(8,128)(2,1)S(1)}, bf16[128,256]{1,0:T(8,128)(2,1)S(1)}, u32[]{:S(2)}, u32[]{:S(2)}) collective-permute-start(bf16[128,256]{1,0:T(8,128)(2,1)S(1)} %select_convert_fusion.4), channel_id=1, source_target_pairs={{0,2},{2,0},{4,6},{6,4},{8,10},{10,8},{12,14},{14,12},{1,3},{3,1},... | collective-permute-start | bytes 196616 | tf_op jit(solution)/shard_map/ppermute | solution.py:28
  14.1 25.9 %copy-start.1 = (bf16[512,4096]{1,0:T(8,128)(2,1)S(1)}, bf16[512,4096]{1,0:T(8,128)(2,1)}, u32[]{:S(2)}) copy-start(bf16[512,4096]{1,0:T(8,128)(2,1)} %slab_ref.3) | copy-start | bytes 12582916
  14.1 6.7 %collective-permute-start.11 = (bf16[128,256]{1,0:T(8,128)(2,1)S(1)}, bf16[128,256]{1,0:T(8,128)(2,1)S(1)}, u32[]{:S(2)}, u32[]{:S(2)}) collective-permute-start(bf16[128,256]{1,0:T(8,128)(2,1)S(1)} %select_convert_fusion.5), channel_id=1, source_target_pairs={{0,4},{2,6},{4,0},{6,2},{8,12},{10,14},{12,8},{14,10},{1,5},{3,7},... | collective-permute-start | bytes 196616 | tf_op jit(solution)/shard_map/ppermute | solution.py:28
  16.0 5.8 %collective-permute-start.6 = (bf16[128,256]{1,0:T(8,128)(2,1)S(1)}, bf16[128,256]{1,0:T(8,128)(2,1)S(1)}, u32[]{:S(2)}, u32[]{:S(2)}) collective-permute-start(bf16[128,256]{1,0:T(8,128)(2,1)S(1)} %select_convert_fusion.6), channel_id=1, source_target_pairs={{0,2},{2,0},{4,6},{6,4},{8,10},{10,8},{12,14},{14,12},{1,3},{3,1},... | collective-permute-start | bytes 196616 | tf_op jit(solution)/shard_map/ppermute | solution.py:28
  16.7 7.3 %collective-permute-start.1 = (bf16[128,256]{1,0:T(8,128)(2,1)S(1)}, bf16[128,256]{1,0:T(8,128)(2,1)S(1)}, u32[]{:S(2)}, u32[]{:S(2)}) collective-permute-start(bf16[128,256]{1,0:T(8,128)(2,1)S(1)} %select_convert_fusion.7), channel_id=1, source_target_pairs={{0,4},{2,6},{4,0},{6,2},{8,12},{10,14},{12,8},{14,10},{1,5},{3,7},... | collective-permute-start | bytes 196616 | tf_op jit(solution)/shard_map/ppermute | solution.py:28
  18.2 8.8 %collective-permute-start.17 = (bf16[128,256]{1,0:T(8,128)(2,1)S(1)}, bf16[128,256]{1,0:T(8,128)(2,1)S(1)}, u32[]{:S(2)}, u32[]{:S(2)}) collective-permute-start(bf16[128,256]{1,0:T(8,128)(2,1)S(1)} %fusion.27), channel_id=1, source_target_pairs={{0,8},{2,10},{4,12},{6,14},{8,0},{10,2},{12,4},{14,6},{1,9},{3,11}... | collective-permute-start | bytes 196616 | tf_op jit(solution)/shard_map/ppermute | solution.py:28
  20.9 9.1 %collective-permute-start.12 = (bf16[128,256]{1,0:T(8,128)(2,1)S(1)}, bf16[128,256]{1,0:T(8,128)(2,1)S(1)}, u32[]{:S(2)}, u32[]{:S(2)}) collective-permute-start(bf16[128,256]{1,0:T(8,128)(2,1)S(1)} %fusion.26), channel_id=1, source_target_pairs={{0,8},{2,10},{4,12},{6,14},{8,0},{10,2},{12,4},{14,6},{1,9},{3,11}... | collective-permute-start | bytes 196616 | tf_op jit(solution)/shard_map/ppermute | solution.py:28
  21.8 9.3 %collective-permute-start.7 = (bf16[128,256]{1,0:T(8,128)(2,1)S(1)}, bf16[128,256]{1,0:T(8,128)(2,1)S(1)}, u32[]{:S(2)}, u32[]{:S(2)}) collective-permute-start(bf16[128,256]{1,0:T(8,128)(2,1)S(1)} %fusion.25), channel_id=1, source_target_pairs={{0,8},{2,10},{4,12},{6,14},{8,0},{10,2},{12,4},{14,6},{1,9},{3,11}... | collective-permute-start | bytes 196616 | tf_op jit(solution)/shard_map/ppermute | solution.py:28
  24.0 8.3 %collective-permute-start.2 = (bf16[128,256]{1,0:T(8,128)(2,1)S(1)}, bf16[128,256]{1,0:T(8,128)(2,1)S(1)}, u32[]{:S(2)}, u32[]{:S(2)}) collective-permute-start(bf16[128,256]{1,0:T(8,128)(2,1)S(1)} %fusion.24), channel_id=1, source_target_pairs={{0,8},{2,10},{4,12},{6,14},{8,0},{10,2},{12,4},{14,6},{1,9},{3,11}... | collective-permute-start | bytes 196616 | tf_op jit(solution)/shard_map/ppermute | solution.py:28
  27.1 6.4 %collective-permute-start.18 = (bf16[128,256]{1,0:T(8,128)(2,1)S(1)}, bf16[128,256]{1,0:T(8,128)(2,1)S(1)}, u32[]{:S(2)}, u32[]{:S(2)}) collective-permute-start(bf16[128,256]{1,0:T(8,128)(2,1)S(1)} %multiply_convert_fusion), channel_id=1, source_target_pairs={{0,2},{2,0},{4,6},{6,4},{8,10},{10,8},{12,14},{14,12},{1,3},{3,1},... | collective-permute-start | bytes 196616 | tf_op jit(solution)/shard_map/ppermute | solution.py:28
  30.0 5.0 %collective-permute-start.13 = (bf16[128,256]{1,0:T(8,128)(2,1)S(1)}, bf16[128,256]{1,0:T(8,128)(2,1)S(1)}, u32[]{:S(2)}, u32[]{:S(2)}) collective-permute-start(bf16[128,256]{1,0:T(8,128)(2,1)S(1)} %multiply_convert_fusion.1), channel_id=1, source_target_pairs={{0,4},{2,6},{4,0},{6,2},{8,12},{10,14},{12,8},{14,10},{1,5},{3,7},... | collective-permute-start | bytes 196616 | tf_op jit(solution)/shard_map/ppermute | solution.py:28
  31.1 5.2 %collective-permute-start.8 = (bf16[128,256]{1,0:T(8,128)(2,1)S(1)}, bf16[128,256]{1,0:T(8,128)(2,1)S(1)}, u32[]{:S(2)}, u32[]{:S(2)}) collective-permute-start(bf16[128,256]{1,0:T(8,128)(2,1)S(1)} %multiply_convert_fusion.2), channel_id=1, source_target_pairs={{0,2},{2,0},{4,6},{6,4},{8,10},{10,8},{12,14},{14,12},{1,3},{3,1},... | collective-permute-start | bytes 196616 | tf_op jit(solution)/shard_map/ppermute | solution.py:28
  32.3 5.1 %collective-permute-start.3 = (bf16[128,256]{1,0:T(8,128)(2,1)S(1)}, bf16[128,256]{1,0:T(8,128)(2,1)S(1)}, u32[]{:S(2)}, u32[]{:S(2)}) collective-permute-start(bf16[128,256]{1,0:T(8,128)(2,1)S(1)} %multiply_convert_fusion.3), channel_id=1, source_target_pairs={{0,4},{2,6},{4,0},{6,2},{8,12},{10,14},{12,8},{14,10},{1,5},{3,7},... | collective-permute-start | bytes 196616 | tf_op jit(solution)/shard_map/ppermute | solution.py:28
  33.5 6.4 %collective-permute-start.19 = (bf16[128,512]{1,0:T(8,128)(2,1)S(1)}, bf16[128,512]{1,0:T(8,128)(2,1)S(1)}, u32[]{:S(2)}, u32[]{:S(2)}) collective-permute-start(bf16[128,512]{1,0:T(8,128)(2,1)S(1)} %pad_maximum_fusion.4), channel_id=1, source_target_pairs={{0,4},{2,6},{4,0},{6,2},{8,12},{10,14},{12,8},{14,10},{1,5},{3,7},... | collective-permute-start | bytes 393224 | tf_op jit(solution)/shard_map/ppermute | solution.py:28
  35.1 5.6 %collective-permute-start.14 = (bf16[128,512]{1,0:T(8,128)(2,1)S(1)}, bf16[128,512]{1,0:T(8,128)(2,1)S(1)}, u32[]{:S(2)}, u32[]{:S(2)}) collective-permute-start(bf16[128,512]{1,0:T(8,128)(2,1)S(1)} %pad_maximum_fusion.3), channel_id=1, source_target_pairs={{0,2},{2,0},{4,6},{6,4},{8,10},{10,8},{12,14},{14,12},{1,3},{3,1},... | collective-permute-start | bytes 393224 | tf_op jit(solution)/shard_map/ppermute | solution.py:28
  36.3 5.0 %collective-permute-start.9 = (bf16[128,512]{1,0:T(8,128)(2,1)S(1)}, bf16[128,512]{1,0:T(8,128)(2,1)S(1)}, u32[]{:S(2)}, u32[]{:S(2)}) collective-permute-start(bf16[128,512]{1,0:T(8,128)(2,1)S(1)} %pad_maximum_fusion.2), channel_id=1, source_target_pairs={{0,4},{2,6},{4,0},{6,2},{8,12},{10,14},{12,8},{14,10},{1,5},{3,7},... | collective-permute-start | bytes 393224 | tf_op jit(solution)/shard_map/ppermute | solution.py:28
  37.5 5.0 %collective-permute-start.4 = (bf16[128,512]{1,0:T(8,128)(2,1)S(1)}, bf16[128,512]{1,0:T(8,128)(2,1)S(1)}, u32[]{:S(2)}, u32[]{:S(2)}) collective-permute-start(bf16[128,512]{1,0:T(8,128)(2,1)S(1)} %pad_maximum_fusion.1), channel_id=1, source_target_pairs={{0,2},{2,0},{4,6},{6,4},{8,10},{10,8},{12,14},{14,12},{1,3},{3,1},... | collective-permute-start | bytes 393224 | tf_op jit(solution)/shard_map/ppermute | solution.py:28
  43.0 1.6 %collective-permute-start.20 = (f32[512,128]{1,0:T(8,128)S(1)}, f32[512,128]{1,0:T(8,128)S(1)}, u32[]{:S(2)}, u32[]{:S(2)}) collective-permute-start(f32[512,128]{1,0:T(8,128)S(1)} %fusion.2.mine_ref), channel_id=1, source_target_pairs={{0,1},{1,0},{2,3},{3,2},{4,5},{5,4},{6,7},{7,6},{8,9},{9,8},{10,11... | collective-permute-start | bytes 786440 | tf_op jit(solution)/shard_map/ppermute | solution.py:28
  45.1 4.2 %collective-permute-start.23 = (f32[72,128]{1,0:T(8,128)S(1)}, f32[72,128]{1,0:T(8,128)S(1)}, u32[]{:S(2)}, u32[]{:S(2)}) collective-permute-start(f32[72,128]{1,0:T(8,128)S(1)} %make_gram.1), channel_id=1, source_target_pairs={{0,4},{1,13},{2,6},{3,15},{4,0},{5,9},{6,2},{7,11},{8,12},{9,5},{1... | collective-permute-start | bytes 110600 | tf_op jit(solution)/shard_map/ppermute | solution.py:45
  46.2 4.9 %collective-permute-start.24 = (f32[72,128]{1,0:T(8,128)S(1)}, f32[72,128]{1,0:T(8,128)S(1)}, u32[]{:S(2)}, u32[]{:S(2)}) collective-permute-start(f32[72,128]{1,0:T(8,128)S(1)} %make_gram.1), channel_id=1, source_target_pairs={{0,6},{1,15},{2,4},{3,13},{4,2},{5,11},{6,0},{7,9},{8,14},{9,7},{1... | collective-permute-start | bytes 110600 | tf_op jit(solution)/shard_map/ppermute | solution.py:45
  47.6 4.0 %collective-permute-start.22 = (f32[72,128]{1,0:T(8,128)S(1)}, f32[72,128]{1,0:T(8,128)S(1)}, u32[]{:S(2)}, u32[]{:S(2)}) collective-permute-start(f32[72,128]{1,0:T(8,128)S(1)} %make_gram.1), channel_id=1, source_target_pairs={{0,2},{1,11},{2,0},{3,9},{4,6},{5,15},{6,4},{7,13},{8,10},{9,3},{1... | collective-permute-start | bytes 110600 | tf_op jit(solution)/shard_map/ppermute | solution.py:45
  48.6 2.9 %collective-permute-start.21 = (f32[72,128]{1,0:T(8,128)S(1)}, f32[72,128]{1,0:T(8,128)S(1)}, u32[]{:S(2)}, u32[]{:S(2)}) collective-permute-start(f32[72,128]{1,0:T(8,128)S(1)} %make_gram.1), channel_id=1, source_target_pairs={{1,9},{3,11},{5,13},{7,15},{9,1},{11,3},{13,5},{15,7},{17,25},{19,... | collective-permute-start | bytes 110600 | tf_op jit(solution)/shard_map/ppermute | solution.py:45
  51.6 4.4 %collective-permute-start.25 = (f32[72,128]{1,0:T(8,128)S(1)}, f32[72,128]{1,0:T(8,128)S(1)}, u32[]{:S(2)}, u32[]{:S(2)}) collective-permute-start(f32[72,128]{1,0:T(8,128)S(1)} %add_add_fusion), channel_id=1, source_target_pairs={{0,1},{1,0},{2,3},{3,2},{4,5},{5,4},{6,7},{7,6},{8,9},{9,8},{10,11... | collective-permute-start | bytes 110600 | tf_op jit(solution)/shard_map/ppermute | solution.py:28
  60.8 9.2 %collective-permute-start.30 = (bf16[4,16,2048]{2,1,0:T(8,128)(2,1)S(1)}, bf16[4,16,2048]{2,1,0:T(8,128)(2,1)S(1)}, u32[]{:S(2)}, u32[]{:S(2)}) collective-permute-start(bf16[4,16,2048]{2,1,0:T(8,128)(2,1)S(1)} %fusion.11), channel_id=1, source_target_pairs={{0,2},{2,0},{4,6},{6,4},{8,10},{10,8},{12,14},{14,12},{1,3},{3,1},... | collective-permute-start | bytes 786440 | tf_op jit(solution)/shard_map/ppermute | solution.py:28
  61.9 13.2 %collective-permute-start.26 = (bf16[4,16,2048]{2,1,0:T(8,128)(2,1)S(1)}, bf16[4,16,2048]{2,1,0:T(8,128)(2,1)S(1)}, u32[]{:S(2)}, u32[]{:S(2)}) collective-permute-start(bf16[4,16,2048]{2,1,0:T(8,128)(2,1)S(1)} %fusion.10), channel_id=1, source_target_pairs={{0,2},{2,0},{4,6},{6,4},{8,10},{10,8},{12,14},{14,12},{1,3},{3,1},... | collective-permute-start | bytes 786440 | tf_op jit(solution)/shard_map/ppermute | solution.py:28
  70.1 8.7 %collective-permute-start.33 = (bf16[1,16,2048]{2,1,0:T(8,128)(2,1)S(1)}, bf16[1,16,2048]{2,1,0:T(8,128)(2,1)S(1)}, u32[]{:S(2)}, u32[]{:S(2)}) collective-permute-start(bf16[1,16,2048]{2,1,0:T(8,128)(2,1)S(1)} %get-tuple-element.20), channel_id=1, source_target_pairs={{0,12},{2,14},{4,8},{6,10},{8,4},{10,6},{12,0},{14,2},{1,13},{3,15... | collective-permute-start | bytes 196616 | tf_op jit(solution)/shard_map/ppermute | solution.py:28
  72.1 7.6 %collective-permute-start.32 = (bf16[1,16,2048]{2,1,0:T(8,128)(2,1)S(1)}, bf16[1,16,2048]{2,1,0:T(8,128)(2,1)S(1)}, u32[]{:S(2)}, u32[]{:S(2)}) collective-permute-start(bf16[1,16,2048]{2,1,0:T(8,128)(2,1)S(1)} %get-tuple-element.21), channel_id=1, source_target_pairs={{0,8},{2,10},{4,12},{6,14},{8,0},{10,2},{12,4},{14,6},{1,9},{3,11}... | collective-permute-start | bytes 196616 | tf_op jit(solution)/shard_map/ppermute | solution.py:28
  73.8 5.8 %collective-permute-start.31 = (bf16[1,16,2048]{2,1,0:T(8,128)(2,1)S(1)}, bf16[1,16,2048]{2,1,0:T(8,128)(2,1)S(1)}, u32[]{:S(2)}, u32[]{:S(2)}) collective-permute-start(bf16[1,16,2048]{2,1,0:T(8,128)(2,1)S(1)} %get-tuple-element.19), channel_id=1, source_target_pairs={{0,4},{2,6},{4,0},{6,2},{8,12},{10,14},{12,8},{14,10},{1,5},{3,7},... | collective-permute-start | bytes 196616 | tf_op jit(solution)/shard_map/ppermute | solution.py:28
  75.2 6.9 %collective-permute-start.29 = (bf16[1,16,2048]{2,1,0:T(8,128)(2,1)S(1)}, bf16[1,16,2048]{2,1,0:T(8,128)(2,1)S(1)}, u32[]{:S(2)}, u32[]{:S(2)}) collective-permute-start(bf16[1,16,2048]{2,1,0:T(8,128)(2,1)S(1)} %get-tuple-element.17), channel_id=1, source_target_pairs={{0,12},{2,14},{4,8},{6,10},{8,4},{10,6},{12,0},{14,2},{1,13},{3,15... | collective-permute-start | bytes 196616 | tf_op jit(solution)/shard_map/ppermute | solution.py:28
  77.1 7.5 %collective-permute-start.28 = (bf16[1,16,2048]{2,1,0:T(8,128)(2,1)S(1)}, bf16[1,16,2048]{2,1,0:T(8,128)(2,1)S(1)}, u32[]{:S(2)}, u32[]{:S(2)}) collective-permute-start(bf16[1,16,2048]{2,1,0:T(8,128)(2,1)S(1)} %get-tuple-element.18), channel_id=1, source_target_pairs={{0,8},{2,10},{4,12},{6,14},{8,0},{10,2},{12,4},{14,6},{1,9},{3,11}... | collective-permute-start | bytes 196616 | tf_op jit(solution)/shard_map/ppermute | solution.py:28
  78.9 5.7 %collective-permute-start.27 = (bf16[1,16,2048]{2,1,0:T(8,128)(2,1)S(1)}, bf16[1,16,2048]{2,1,0:T(8,128)(2,1)S(1)}, u32[]{:S(2)}, u32[]{:S(2)}) collective-permute-start(bf16[1,16,2048]{2,1,0:T(8,128)(2,1)S(1)} %get-tuple-element.16), channel_id=1, source_target_pairs={{0,4},{2,6},{4,0},{6,2},{8,12},{10,14},{12,8},{14,10},{1,5},{3,7},... | collective-permute-start | bytes 196616 | tf_op jit(solution)/shard_map/ppermute | solution.py:28

commit v13 on v12

--- a/solution.py
+++ b/solution.py
@@ -9,7 +9,6 @@
 from jax.sharding import PartitionSpec as P
 
 SKETCH_CHUNKS = 4
-CHUNKS = 2
 TILE = 512
 KERNEL_VMEM = 50 * 2**20
 
@@ -35,11 +34,12 @@
     stride = 1
     while stride < rows:
         radix = min(8, rows // stride)
+        split = min(2, radix // 2)
         terms = []
-        for t in range(radix // 2):
+        for near in [digit for digit in range(radix) if not digit & split]:
             pairs = []
             for row in range(rows):
-                for core, digit in ((0, t), (1, t + radix // 2)):
+                for core, digit in ((0, near), (1, near | split)):
                     if digit:
                         pairs.append((row * cores + core, (row ^ digit * stride) * cores + core))
             terms.append(lax.ppermute(value, ("row", "col"), pairs))
@@ -55,21 +55,22 @@
     return lax.rem(lax.div(lax.axis_index(axis), stride), radix)
 
 
-def scatter_level(blocks, axis, stride, radix):
-    digit = digit_of(axis, stride, radix)
-    view = blocks.reshape((blocks.shape[0] // radix, radix) + blocks.shape[1:])
-    total = lax.dynamic_index_in_dim(view, digit, 1, keepdims=False)
-    for t in range(1, radix):
-        part = lax.dynamic_index_in_dim(view, jnp.bitwise_xor(digit, t), 1, keepdims=False)
-        landed = swap(part.astype(jnp.bfloat16), axis, t * stride)
-        total = total + landed.astype(jnp.float32)
-    return total
-
-
-def scatter_sum(blocks, axis):
-    for stride, radix in levels_of(lax.axis_size(axis)):
-        blocks = scatter_level(blocks, axis, stride, radix)
-    return blocks[0]
+def scatter_sum(value, axis, reverse):
+    levels = levels_of(lax.axis_size(axis))
+    rows = value.shape[0] // lax.axis_size(axis)
+    total = value.reshape([radix for _, radix in reversed(levels)] + [rows, value.shape[1]])
+    order = range(len(levels))
+    for level in reversed(order) if reverse else order:
+        stride, radix = levels[level]
+        dim = len(levels) - 1 - level
+        digit = digit_of(axis, stride, radix)
+        parts = total
+        total = lax.dynamic_slice_in_dim(parts, digit, 1, dim)
+        for t in range(1, radix):
+            part = lax.dynamic_slice_in_dim(parts, jnp.bitwise_xor(digit, t), 1, dim)
+            landed = swap(part.astype(jnp.bfloat16), axis, t * stride)
+            total = total + landed.astype(jnp.float32)
+    return total.reshape(rows, value.shape[1])
 
 
 def bit_of(axis, bit):
@@ -314,9 +315,6 @@
     total_cols = cols_here * lax.axis_size("col")
     root_rows = math.sqrt(total_rows)
 
-    cols_chunk = cols_here // CHUNKS
-    spans = [slice(c * cols_chunk, (c + 1) * cols_chunk) for c in range(CHUNKS)]
-
     local_cols = first_product(start_sketch, activations, SKETCH_CHUNKS)
     partial_sketch = 0.0
     orders = orders_of("row")
@@ -336,10 +334,11 @@
         gram, partial_sketch, other_sketch, activations, total_cols, root_rows
     )
 
-    pieces = []
-    for span in spans:
-        blocks = local_proj[:, span].reshape(parts, width // parts, cols_chunk)
-        pieces.append(scatter_sum(blocks, "row") / total_rows)
+    cut = cols_here * 5 // 8
+    pieces = [
+        scatter_sum(local_proj[:, :cut], "row", False) / total_rows,
+        scatter_sum(local_proj[:, cut:], "row", True) / total_rows,
+    ]
     return (basis, jnp.concatenate(pieces, axis=1))
 
 

time: 85.5 us -> 84.6 us (0.989)
  starting transfers between devices: 45.4 us -> 43.3 us
  waiting for transfers between devices: 26.1 us -> 27.4 us
    ppermute x30, starting transfers between devices: 41.2 us -> 38.2 us  [swap(): return lax.ppermute(value, axis, [(i, i ^ distance) for i in range(size)])]
    ppermute x4, waiting for transfers between devices: 2.25 us -> 3.45 us  [row_sum(): terms.append(lax.ppermute(value, ('row', 'col'), pairs))]
    ppermute x4, starting transfers between devices: 4.21 us -> 5.1 us  [row_sum(): terms.append(lax.ppermute(value, ('row', 'col'), pairs))]
  transfers between devices with their start and end apart: 34 -> 34, of which waited for: 18 -> 19; matrix products, arithmetic and copies ran while one was open for 3% -> 3% of each run, Pallas kernels for 0% -> 0%
where the time goes in v13:
time: 84.6 us; the launch traced here: 84.5 us
  starting transfers between devices  43.3 us (51%)
  waiting for transfers between devices  27.4 us (32%)
  Pallas kernels  8.12 us (10%)
  other arithmetic  1.79 us (2%)
  matrix products  1.74 us (2%)
  local copies, waits for them, and re-layouts  1.18 us (1%)
  between operations  0.99 us (1%)
    ppermute x30, starting transfers between devices, swap(): return lax.ppermute(value, axis, [(i, i ^ distance) for i in range(size)])  38.2 us
    ppermute x30, waiting for transfers between devices, swap(): return lax.ppermute(value, axis, [(i, i ^ distance) for i in range(size)])  23.9 us
    ppermute x4, starting transfers between devices, row_sum(): terms.append(lax.ppermute(value, ('row', 'col'), pairs))  5.1 us
    pallas_call x1, Pallas kernels, make_basis(): pl.pallas_call(functools.partial(basis_kernel, total_cols, root_rows), ou...  4.63 us
    ppermute x4, waiting for transfers between devices, row_sum(): terms.append(lax.ppermute(value, ('row', 'col'), pairs))  3.45 us
    pallas_call x1, Pallas kernels, first_product(): pl.pallas_call(sketch_kernel, out_shape=[jax.ShapeDtypeStruct((width, col...  3 us
    dot_general x4, matrix products, per_device(): lax.dot_general(activations[:, span], shared, (((1,), (1,)), ((), ())), p...  1.74 us
  transfers between devices with their start and end apart: 34, of which 19 were waited for; matrix products, arithmetic and copies ran while one was open for 3% of the time, Pallas kernels for 0%

profile of v13, /device:TPU:0, one launch (start us, length us, event | category | flops | bytes accessed | tf_op | source)
XLA Modules:
  0.0 84.5 jit_solution(6583405144345583053)
XLA Ops:
  0.7 0.9 %copy-done = bf16[512,128]{1,0:T(8,128)(2,1)S(1)} copy-done((bf16[512,128]{1,0:T(8,128)(2,1)S(1)}, bf16[512,128]{1,0:T(8,128)(2,1)}, u32[]{:S(2)}) %copy-start) | copy-done | bytes 131096
  1.6 3.0 %first_product.1 = (f32[128,1024]{1,0:T(8,128)S(1)}, f32[128,1024]{1,0:T(8,128)S(1)}, f32[128,1024]{1,0:T(8,128)S(1)}, f32[128,1024]{1,0:T(8,128)S(1)}) custom-call(bf16[512,128]{1,0:T(8,128)(2,1)S(1)} %copy-done, bf16[512,4096]{1,0:T(8,128)(2,1)} %slab_ref.3), custom_call_target="tpu_custom_call" | custom-call | flops 536870912 | bytes 4194304 | tf_op jit(solution)/shard_map/first_product/pallas_call | solution.py:133
  4.6 3.1 %collective-permute-start.15 = (bf16[128,512]{1,0:T(8,128)(2,1)S(1)}, bf16[128,512]{1,0:T(8,128)(2,1)S(1)}, u32[]{:S(2)}, u32[]{:S(2)}) collective-permute-start(bf16[128,512]{1,0:T(8,128)(2,1)S(1)} %select_convert_fusion), channel_id=1, source_target_pairs={{0,4},{2,6},{4,0},{6,2},{8,12},{10,14},{12,8},{14,10},{1,5},{3,7},... | collective-permute-start | bytes 393224 | tf_op jit(solution)/shard_map/ppermute | solution.py:27
  7.7 1.6 %collective-permute-start.10 = (bf16[128,512]{1,0:T(8,128)(2,1)S(1)}, bf16[128,512]{1,0:T(8,128)(2,1)S(1)}, u32[]{:S(2)}, u32[]{:S(2)}) collective-permute-start(bf16[128,512]{1,0:T(8,128)(2,1)S(1)} %select_convert_fusion.1), channel_id=1, source_target_pairs={{0,2},{2,0},{4,6},{6,4},{8,10},{10,8},{12,14},{14,12},{1,3},{3,1},... | collective-permute-start | bytes 393224 | tf_op jit(solution)/shard_map/ppermute | solution.py:27
  10.0 1.6 %collective-permute-done.15 = bf16[128,512]{1,0:T(8,128)(2,1)S(1)} collective-permute-done((bf16[128,512]{1,0:T(8,128)(2,1)S(1)}, bf16[128,512]{1,0:T(8,128)(2,1)S(1)}, u32[]{:S(2)}, u32[]{:S(2)}) %collective-permute-start.15) | collective-permute-done | bytes 131104 | tf_op jit(solution)/shard_map/ppermute | solution.py:27
  11.7 2.4 %collective-permute-start.16 = (bf16[128,256]{1,0:T(8,128)(2,1)S(1)}, bf16[128,256]{1,0:T(8,128)(2,1)S(1)}, u32[]{:S(2)}, u32[]{:S(2)}) collective-permute-start(bf16[128,256]{1,0:T(8,128)(2,1)S(1)} %select_convert_fusion.4), channel_id=1, source_target_pairs={{0,2},{2,0},{4,6},{6,4},{8,10},{10,8},{12,14},{14,12},{1,3},{3,1},... | collective-permute-start | bytes 196616 | tf_op jit(solution)/shard_map/ppermute | solution.py:27
  14.1 1.7 %collective-permute-start.11 = (bf16[128,256]{1,0:T(8,128)(2,1)S(1)}, bf16[128,256]{1,0:T(8,128)(2,1)S(1)}, u32[]{:S(2)}, u32[]{:S(2)}) collective-permute-start(bf16[128,256]{1,0:T(8,128)(2,1)S(1)} %select_convert_fusion.5), channel_id=1, source_target_pairs={{0,4},{2,6},{4,0},{6,2},{8,12},{10,14},{12,8},{14,10},{1,5},{3,7},... | collective-permute-start | bytes 196616 | tf_op jit(solution)/shard_map/ppermute | solution.py:27
  16.0 0.6 collective-permute-start.6
  16.7 1.5 %collective-permute-start.1 = (bf16[128,256]{1,0:T(8,128)(2,1)S(1)}, bf16[128,256]{1,0:T(8,128)(2,1)S(1)}, u32[]{:S(2)}, u32[]{:S(2)}) collective-permute-start(bf16[128,256]{1,0:T(8,128)(2,1)S(1)} %select_convert_fusion.7), channel_id=1, source_target_pairs={{0,4},{2,6},{4,0},{6,2},{8,12},{10,14},{12,8},{14,10},{1,5},{3,7},... | collective-permute-start | bytes 196616 | tf_op jit(solution)/shard_map/ppermute | solution.py:27
  18.2 2.6 %collective-permute-start.17 = (bf16[128,256]{1,0:T(8,128)(2,1)S(1)}, bf16[128,256]{1,0:T(8,128)(2,1)S(1)}, u32[]{:S(2)}, u32[]{:S(2)}) collective-permute-start(bf16[128,256]{1,0:T(8,128)(2,1)S(1)} %fusion.25), channel_id=1, source_target_pairs={{0,8},{2,10},{4,12},{6,14},{8,0},{10,2},{12,4},{14,6},{1,9},{3,11}... | collective-permute-start | bytes 196616 | tf_op jit(solution)/shard_map/ppermute | solution.py:27
  20.9 0.9 %collective-permute-start.12 = (bf16[128,256]{1,0:T(8,128)(2,1)S(1)}, bf16[128,256]{1,0:T(8,128)(2,1)S(1)}, u32[]{:S(2)}, u32[]{:S(2)}) collective-permute-start(bf16[128,256]{1,0:T(8,128)(2,1)S(1)} %fusion.24), channel_id=1, source_target_pairs={{0,8},{2,10},{4,12},{6,14},{8,0},{10,2},{12,4},{14,6},{1,9},{3,11}... | collective-permute-start | bytes 196616 | tf_op jit(solution)/shard_map/ppermute | solution.py:27
  21.8 2.2 %collective-permute-start.7 = (bf16[128,256]{1,0:T(8,128)(2,1)S(1)}, bf16[128,256]{1,0:T(8,128)(2,1)S(1)}, u32[]{:S(2)}, u32[]{:S(2)}) collective-permute-start(bf16[128,256]{1,0:T(8,128)(2,1)S(1)} %fusion.23), channel_id=1, source_target_pairs={{0,8},{2,10},{4,12},{6,14},{8,0},{10,2},{12,4},{14,6},{1,9},{3,11}... | collective-permute-start | bytes 196616 | tf_op jit(solution)/shard_map/ppermute | solution.py:27
  24.0 0.9 %collective-permute-start.2 = (bf16[128,256]{1,0:T(8,128)(2,1)S(1)}, bf16[128,256]{1,0:T(8,128)(2,1)S(1)}, u32[]{:S(2)}, u32[]{:S(2)}) collective-permute-start(bf16[128,256]{1,0:T(8,128)(2,1)S(1)} %fusion.22), channel_id=1, source_target_pairs={{0,8},{2,10},{4,12},{6,14},{8,0},{10,2},{12,4},{14,6},{1,9},{3,11}... | collective-permute-start | bytes 196616 | tf_op jit(solution)/shard_map/ppermute | solution.py:27
  24.9 2.2 %collective-permute-done.17 = bf16[128,256]{1,0:T(8,128)(2,1)S(1)} collective-permute-done((bf16[128,256]{1,0:T(8,128)(2,1)S(1)}, bf16[128,256]{1,0:T(8,128)(2,1)S(1)}, u32[]{:S(2)}, u32[]{:S(2)}) %collective-permute-start.17) | collective-permute-done | bytes 65568 | tf_op jit(solution)/shard_map/ppermute | solution.py:27
  27.1 1.8 %collective-permute-start.18 = (bf16[128,256]{1,0:T(8,128)(2,1)S(1)}, bf16[128,256]{1,0:T(8,128)(2,1)S(1)}, u32[]{:S(2)}, u32[]{:S(2)}) collective-permute-start(bf16[128,256]{1,0:T(8,128)(2,1)S(1)} %multiply_convert_fusion), channel_id=1, source_target_pairs={{0,2},{2,0},{4,6},{6,4},{8,10},{10,8},{12,14},{14,12},{1,3},{3,1},... | collective-permute-start | bytes 196616 | tf_op jit(solution)/shard_map/ppermute | solution.py:27
  28.9 1.1 %collective-permute-done.12 = bf16[128,256]{1,0:T(8,128)(2,1)S(1)} collective-permute-done((bf16[128,256]{1,0:T(8,128)(2,1)S(1)}, bf16[128,256]{1,0:T(8,128)(2,1)S(1)}, u32[]{:S(2)}, u32[]{:S(2)}) %collective-permute-start.12) | collective-permute-done | bytes 65568 | tf_op jit(solution)/shard_map/ppermute | solution.py:27
  30.1 1.0 %collective-permute-done.7 = bf16[128,256]{1,0:T(8,128)(2,1)S(1)} collective-permute-done((bf16[128,256]{1,0:T(8,128)(2,1)S(1)}, bf16[128,256]{1,0:T(8,128)(2,1)S(1)}, u32[]{:S(2)}, u32[]{:S(2)}) %collective-permute-start.7) | collective-permute-done | bytes 65568 | tf_op jit(solution)/shard_map/ppermute | solution.py:27
  31.1 1.2 %collective-permute-start.8 = (bf16[128,256]{1,0:T(8,128)(2,1)S(1)}, bf16[128,256]{1,0:T(8,128)(2,1)S(1)}, u32[]{:S(2)}, u32[]{:S(2)}) collective-permute-start(bf16[128,256]{1,0:T(8,128)(2,1)S(1)} %multiply_convert_fusion.2), channel_id=1, source_target_pairs={{0,2},{2,0},{4,6},{6,4},{8,10},{10,8},{12,14},{14,12},{1,3},{3,1},... | collective-permute-start | bytes 196616 | tf_op jit(solution)/shard_map/ppermute | solution.py:27
  32.3 1.1 %collective-permute-start.3 = (bf16[128,256]{1,0:T(8,128)(2,1)S(1)}, bf16[128,256]{1,0:T(8,128)(2,1)S(1)}, u32[]{:S(2)}, u32[]{:S(2)}) collective-permute-start(bf16[128,256]{1,0:T(8,128)(2,1)S(1)} %multiply_convert_fusion.3), channel_id=1, source_target_pairs={{0,4},{2,6},{4,0},{6,2},{8,12},{10,14},{12,8},{14,10},{1,5},{3,7},... | collective-permute-start | bytes 196616 | tf_op jit(solution)/shard_map/ppermute | solution.py:27
  33.5 1.0 %collective-permute-start.19 = (bf16[128,512]{1,0:T(8,128)(2,1)S(1)}, bf16[128,512]{1,0:T(8,128)(2,1)S(1)}, u32[]{:S(2)}, u32[]{:S(2)}) collective-permute-start(bf16[128,512]{1,0:T(8,128)(2,1)S(1)} %pad_maximum_fusion.4), channel_id=1, source_target_pairs={{0,4},{2,6},{4,0},{6,2},{8,12},{10,14},{12,8},{14,10},{1,5},{3,7},... | collective-permute-start | bytes 393224 | tf_op jit(solution)/shard_map/ppermute | solution.py:27
  35.1 1.2 %collective-permute-start.14 = (bf16[128,512]{1,0:T(8,128)(2,1)S(1)}, bf16[128,512]{1,0:T(8,128)(2,1)S(1)}, u32[]{:S(2)}, u32[]{:S(2)}) collective-permute-start(bf16[128,512]{1,0:T(8,128)(2,1)S(1)} %pad_maximum_fusion.3), channel_id=1, source_target_pairs={{0,2},{2,0},{4,6},{6,4},{8,10},{10,8},{12,14},{14,12},{1,3},{3,1},... | collective-permute-start | bytes 393224 | tf_op jit(solution)/shard_map/ppermute | solution.py:27
  36.3 0.9 %collective-permute-start.9 = (bf16[128,512]{1,0:T(8,128)(2,1)S(1)}, bf16[128,512]{1,0:T(8,128)(2,1)S(1)}, u32[]{:S(2)}, u32[]{:S(2)}) collective-permute-start(bf16[128,512]{1,0:T(8,128)(2,1)S(1)} %pad_maximum_fusion.2), channel_id=1, source_target_pairs={{0,4},{2,6},{4,0},{6,2},{8,12},{10,14},{12,8},{14,10},{1,5},{3,7},... | collective-permute-start | bytes 393224 | tf_op jit(solution)/shard_map/ppermute | solution.py:27
  37.5 1.1 %collective-permute-start.4 = (bf16[128,512]{1,0:T(8,128)(2,1)S(1)}, bf16[128,512]{1,0:T(8,128)(2,1)S(1)}, u32[]{:S(2)}, u32[]{:S(2)}) collective-permute-start(bf16[128,512]{1,0:T(8,128)(2,1)S(1)} %pad_maximum_fusion.1), channel_id=1, source_target_pairs={{0,2},{2,0},{4,6},{6,4},{8,10},{10,8},{12,14},{14,12},{1,3},{3,1},... | collective-permute-start | bytes 393224 | tf_op jit(solution)/shard_map/ppermute | solution.py:27
  38.5 1.4 %collective-permute-done.19 = bf16[128,512]{1,0:T(8,128)(2,1)S(1)} collective-permute-done((bf16[128,512]{1,0:T(8,128)(2,1)S(1)}, bf16[128,512]{1,0:T(8,128)(2,1)S(1)}, u32[]{:S(2)}, u32[]{:S(2)}) %collective-permute-start.19) | collective-permute-done | bytes 131104 | tf_op jit(solution)/shard_map/ppermute | solution.py:27
  41.9 0.6 collective-permute-done.4
  43.1 1.5 %collective-permute-done.20.other_ref = f32[512,128]{1,0:T(8,128)S(1)} collective-permute-done((f32[512,128]{1,0:T(8,128)S(1)}, f32[512,128]{1,0:T(8,128)S(1)}, u32[]{:S(2)}, u32[]{:S(2)}) %collective-permute-start.20) | collective-permute-done | bytes 262176 | tf_op jit(solution)/shard_map/ppermute | solution.py:27
  45.1 1.9 %collective-permute-start.23 = (f32[72,128]{1,0:T(8,128)S(1)}, f32[72,128]{1,0:T(8,128)S(1)}, u32[]{:S(2)}, u32[]{:S(2)}) collective-permute-start(f32[72,128]{1,0:T(8,128)S(1)} %make_gram.1), channel_id=1, source_target_pairs={{0,8},{1,13},{2,10},{3,15},{4,12},{5,9},{6,14},{7,11},{8,0},{9,5},... | collective-permute-start | bytes 110600 | tf_op jit(solution)/shard_map/ppermute | solution.py:45
  47.0 1.5 %collective-permute-start.24 = (f32[72,128]{1,0:T(8,128)S(1)}, f32[72,128]{1,0:T(8,128)S(1)}, u32[]{:S(2)}, u32[]{:S(2)}) collective-permute-start(f32[72,128]{1,0:T(8,128)S(1)} %make_gram.1), channel_id=1, source_target_pairs={{0,10},{1,15},{2,8},{3,13},{4,14},{5,11},{6,12},{7,9},{8,2},{9,7},... | collective-permute-start | bytes 110600 | tf_op jit(solution)/shard_map/ppermute | solution.py:45
  48.5 1.0 %collective-permute-start.22 = (f32[72,128]{1,0:T(8,128)S(1)}, f32[72,128]{1,0:T(8,128)S(1)}, u32[]{:S(2)}, u32[]{:S(2)}) collective-permute-start(f32[72,128]{1,0:T(8,128)S(1)} %make_gram.1), channel_id=1, source_target_pairs={{0,2},{1,7},{2,0},{3,5},{4,6},{5,3},{6,4},{7,1},{8,10},{9,15},{10,... | collective-permute-start | bytes 110600 | tf_op jit(solution)/shard_map/ppermute | solution.py:45
  49.5 0.7 collective-permute-start.21
  50.2 0.9 %collective-permute-done.23 = f32[72,128]{1,0:T(8,128)S(1)} collective-permute-done((f32[72,128]{1,0:T(8,128)S(1)}, f32[72,128]{1,0:T(8,128)S(1)}, u32[]{:S(2)}, u32[]{:S(2)}) %collective-permute-start.23) | collective-permute-done | bytes 36896 | tf_op jit(solution)/shard_map/ppermute | solution.py:45
  51.1 2.3 %collective-permute-done.24 = f32[72,128]{1,0:T(8,128)S(1)} collective-permute-done((f32[72,128]{1,0:T(8,128)S(1)}, f32[72,128]{1,0:T(8,128)S(1)}, u32[]{:S(2)}, u32[]{:S(2)}) %collective-permute-start.24) | collective-permute-done | bytes 36896 | tf_op jit(solution)/shard_map/ppermute | solution.py:45
  53.7 0.6 collective-permute-start.25
  54.2 0.9 %collective-permute-done.25 = f32[72,128]{1,0:T(8,128)S(1)} collective-permute-done((f32[72,128]{1,0:T(8,128)S(1)}, f32[72,128]{1,0:T(8,128)S(1)}, u32[]{:S(2)}, u32[]{:S(2)}) %collective-permute-start.25) | collective-permute-done | bytes 36896 | tf_op jit(solution)/shard_map/ppermute | solution.py:27
  55.1 4.6 %make_basis.1 = (f32[512,128]{1,0:T(8,128)}, f32[128,4096]{1,0:T(8,128)S(1)}) custom-call(f32[72,128]{1,0:T(8,128)S(1)} %add.128.gram_ref, f32[512,128]{1,0:T(8,128)S(1)} %fusion.2.mine_ref, f32[512,128]{1,0:T(8,128)S(1)} %collective-permute-done.20.other_ref, bf16[512,4096]{1,0:T(8,128)(2,1)} %slab_ref.3), custom_call_target="tpu_custom_call" | custom-call | tf_op jit(solution)/shard_map/make_basis/pallas_call | solution.py:290
  60.0 1.9 %collective-permute-start.32 = (bf16[1,2,16,1536]{3,2,1,0:T(8,128)(2,1)S(1)}, bf16[1,2,16,1536]{3,2,1,0:T(8,128)(2,1)S(1)}, u32[]{:S(2)}, u32[]{:S(2)}) collective-permute-start(bf16[1,2,16,1536]{3,2,1,0:T(8,128)(2,1)S(1)} %get-tuple-element.15), channel_id=1, source_target_pairs={{0,12},{2,14},{4,8},{6,10},{8,4},{10,6},{12,0},{14,2},{1,13},{3,15... | collective-permute-start | bytes 294920 | tf_op jit(solution)/shard_map/ppermute | solution.py:27
  61.9 1.3 %collective-permute-start.31 = (bf16[1,2,16,1536]{3,2,1,0:T(8,128)(2,1)S(1)}, bf16[1,2,16,1536]{3,2,1,0:T(8,128)(2,1)S(1)}, u32[]{:S(2)}, u32[]{:S(2)}) collective-permute-start(bf16[1,2,16,1536]{3,2,1,0:T(8,128)(2,1)S(1)} %get-tuple-element.16), channel_id=1, source_target_pairs={{0,8},{2,10},{4,12},{6,14},{8,0},{10,2},{12,4},{14,6},{1,9},{3,11}... | collective-permute-start | bytes 294920 | tf_op jit(solution)/shard_map/ppermute | solution.py:27
  63.2 1.2 %collective-permute-start.30 = (bf16[1,2,16,1536]{3,2,1,0:T(8,128)(2,1)S(1)}, bf16[1,2,16,1536]{3,2,1,0:T(8,128)(2,1)S(1)}, u32[]{:S(2)}, u32[]{:S(2)}) collective-permute-start(bf16[1,2,16,1536]{3,2,1,0:T(8,128)(2,1)S(1)} %get-tuple-element.14), channel_id=1, source_target_pairs={{0,4},{2,6},{4,0},{6,2},{8,12},{10,14},{12,8},{14,10},{1,5},{3,7},... | collective-permute-start | bytes 294920 | tf_op jit(solution)/shard_map/ppermute | solution.py:27
  64.5 1.1 %collective-permute-start.26 = (bf16[4,1,16,2560]{3,2,1,0:T(8,128)(2,1)S(1)}, bf16[4,1,16,2560]{3,2,1,0:T(8,128)(2,1)S(1)}, u32[]{:S(2)}, u32[]{:S(2)}) collective-permute-start(bf16[4,1,16,2560]{3,2,1,0:T(8,128)(2,1)S(1)} %dynamic-slice_convert_fusion), channel_id=1, source_target_pairs={{0,2},{2,0},{4,6},{6,4},{8,10},{10,8},{12,14},{14,12},{1,3},{3,1},... | collective-permute-start | bytes 983048 | tf_op jit(solution)/shard_map/ppermute | solution.py:27
  65.5 2.0 %collective-permute-done.32 = bf16[1,2,16,1536]{3,2,1,0:T(8,128)(2,1)S(1)} collective-permute-done((bf16[1,2,16,1536]{3,2,1,0:T(8,128)(2,1)S(1)}, bf16[1,2,16,1536]{3,2,1,0:T(8,128)(2,1)S(1)}, u32[]{:S(2)}, u32[]{:S(2)}) %collective-permute-start.32) | collective-permute-done | bytes 98336 | tf_op jit(solution)/shard_map/ppermute | solution.py:27
  67.5 5.0 %collective-permute-done.31 = bf16[1,2,16,1536]{3,2,1,0:T(8,128)(2,1)S(1)} collective-permute-done((bf16[1,2,16,1536]{3,2,1,0:T(8,128)(2,1)S(1)}, bf16[1,2,16,1536]{3,2,1,0:T(8,128)(2,1)S(1)}, u32[]{:S(2)}, u32[]{:S(2)}) %collective-permute-start.31) | collective-permute-done | bytes 98336 | tf_op jit(solution)/shard_map/ppermute | solution.py:27
  72.6 1.1 %collective-permute-start.33 = (bf16[1,1,16,1536]{3,2,1,0:T(8,128)(2,1)S(1)}, bf16[1,1,16,1536]{3,2,1,0:T(8,128)(2,1)S(1)}, u32[]{:S(2)}, u32[]{:S(2)}) collective-permute-start(bf16[1,1,16,1536]{3,2,1,0:T(8,128)(2,1)S(1)} %dynamic-slice_convert_fusion.7), channel_id=1, source_target_pairs={{0,2},{2,0},{4,6},{6,4},{8,10},{10,8},{12,14},{14,12},{1,3},{3,1},... | collective-permute-start | bytes 147464 | tf_op jit(solution)/shard_map/ppermute | solution.py:27
  73.8 1.9 %collective-permute-start.29 = (bf16[1,1,16,2560]{3,2,1,0:T(8,128)(2,1)S(1)}, bf16[1,1,16,2560]{3,2,1,0:T(8,128)(2,1)S(1)}, u32[]{:S(2)}, u32[]{:S(2)}) collective-permute-start(bf16[1,1,16,2560]{3,2,1,0:T(8,128)(2,1)S(1)} %get-tuple-element.18), channel_id=1, source_target_pairs={{0,12},{2,14},{4,8},{6,10},{8,4},{10,6},{12,0},{14,2},{1,13},{3,15... | collective-permute-start | bytes 245768 | tf_op jit(solution)/shard_map/ppermute | solution.py:27
  75.7 0.9 %collective-permute-start.28 = (bf16[1,1,16,2560]{3,2,1,0:T(8,128)(2,1)S(1)}, bf16[1,1,16,2560]{3,2,1,0:T(8,128)(2,1)S(1)}, u32[]{:S(2)}, u32[]{:S(2)}) collective-permute-start(bf16[1,1,16,2560]{3,2,1,0:T(8,128)(2,1)S(1)} %get-tuple-element.19), channel_id=1, source_target_pairs={{0,8},{2,10},{4,12},{6,14},{8,0},{10,2},{12,4},{14,6},{1,9},{3,11}... | collective-permute-start | bytes 245768 | tf_op jit(solution)/shard_map/ppermute | solution.py:27
  76.6 1.7 %collective-permute-start.27 = (bf16[1,1,16,2560]{3,2,1,0:T(8,128)(2,1)S(1)}, bf16[1,1,16,2560]{3,2,1,0:T(8,128)(2,1)S(1)}, u32[]{:S(2)}, u32[]{:S(2)}) collective-permute-start(bf16[1,1,16,2560]{3,2,1,0:T(8,128)(2,1)S(1)} %get-tuple-element.17), channel_id=1, source_target_pairs={{0,4},{2,6},{4,0},{6,2},{8,12},{10,14},{12,8},{14,10},{1,5},{3,7},... | collective-permute-start | bytes 245768 | tf_op jit(solution)/shard_map/ppermute | solution.py:27
  78.3 2.8 %collective-permute-done.29 = bf16[1,1,16,2560]{3,2,1,0:T(8,128)(2,1)S(1)} collective-permute-done((bf16[1,1,16,2560]{3,2,1,0:T(8,128)(2,1)S(1)}, bf16[1,1,16,2560]{3,2,1,0:T(8,128)(2,1)S(1)}, u32[]{:S(2)}, u32[]{:S(2)}) %collective-permute-start.29) | collective-permute-done | bytes 81952 | tf_op jit(solution)/shard_map/ppermute | solution.py:27
  81.1 2.6 %collective-permute-done.28 = bf16[1,1,16,2560]{3,2,1,0:T(8,128)(2,1)S(1)} collective-permute-done((bf16[1,1,16,2560]{3,2,1,0:T(8,128)(2,1)S(1)}, bf16[1,1,16,2560]{3,2,1,0:T(8,128)(2,1)S(1)}, u32[]{:S(2)}, u32[]{:S(2)}) %collective-permute-start.28) | collective-permute-done | bytes 81952 | tf_op jit(solution)/shard_map/ppermute | solution.py:27
  83.7 0.7 pad_maximum_fusion
  (76 shorter events, 5.8 us)
Async XLA Ops:
  0.6 0.9 %copy-start = (bf16[512,128]{1,0:T(8,128)(2,1)S(1)}, bf16[512,128]{1,0:T(8,128)(2,1)}, u32[]{:S(2)}) copy-start(bf16[512,128]{1,0:T(8,128)(2,1)} %start_ref.1) | copy-start | bytes 393220
  4.6 7.0 %collective-permute-start.15 = (bf16[128,512]{1,0:T(8,128)(2,1)S(1)}, bf16[128,512]{1,0:T(8,128)(2,1)S(1)}, u32[]{:S(2)}, u32[]{:S(2)}) collective-permute-start(bf16[128,512]{1,0:T(8,128)(2,1)S(1)} %select_convert_fusion), channel_id=1, source_target_pairs={{0,4},{2,6},{4,0},{6,2},{8,12},{10,14},{12,8},{14,10},{1,5},{3,7},... | collective-permute-start | bytes 393224 | tf_op jit(solution)/shard_map/ppermute | solution.py:27
  7.7 6.3 %collective-permute-start.10 = (bf16[128,512]{1,0:T(8,128)(2,1)S(1)}, bf16[128,512]{1,0:T(8,128)(2,1)S(1)}, u32[]{:S(2)}, u32[]{:S(2)}) collective-permute-start(bf16[128,512]{1,0:T(8,128)(2,1)S(1)} %select_convert_fusion.1), channel_id=1, source_target_pairs={{0,2},{2,0},{4,6},{6,4},{8,10},{10,8},{12,14},{14,12},{1,3},{3,1},... | collective-permute-start | bytes 393224 | tf_op jit(solution)/shard_map/ppermute | solution.py:27
  9.3 6.6 %collective-permute-start.5 = (bf16[128,512]{1,0:T(8,128)(2,1)S(1)}, bf16[128,512]{1,0:T(8,128)(2,1)S(1)}, u32[]{:S(2)}, u32[]{:S(2)}) collective-permute-start(bf16[128,512]{1,0:T(8,128)(2,1)S(1)} %select_convert_fusion.2), channel_id=1, source_target_pairs={{0,4},{2,6},{4,0},{6,2},{8,12},{10,14},{12,8},{14,10},{1,5},{3,7},... | collective-permute-start | bytes 393224 | tf_op jit(solution)/shard_map/ppermute | solution.py:27
  9.8 6.7 %collective-permute-start = (bf16[128,512]{1,0:T(8,128)(2,1)S(1)}, bf16[128,512]{1,0:T(8,128)(2,1)S(1)}, u32[]{:S(2)}, u32[]{:S(2)}) collective-permute-start(bf16[128,512]{1,0:T(8,128)(2,1)S(1)} %select_convert_fusion.3), channel_id=1, source_target_pairs={{0,2},{2,0},{4,6},{6,4},{8,10},{10,8},{12,14},{14,12},{1,3},{3,1},... | collective-permute-start | bytes 393224 | tf_op jit(solution)/shard_map/ppermute | solution.py:27
  11.7 6.5 %collective-permute-start.16 = (bf16[128,256]{1,0:T(8,128)(2,1)S(1)}, bf16[128,256]{1,0:T(8,128)(2,1)S(1)}, u32[]{:S(2)}, u32[]{:S(2)}) collective-permute-start(bf16[128,256]{1,0:T(8,128)(2,1)S(1)} %select_convert_fusion.4), channel_id=1, source_target_pairs={{0,2},{2,0},{4,6},{6,4},{8,10},{10,8},{12,14},{14,12},{1,3},{3,1},... | collective-permute-start | bytes 196616 | tf_op jit(solution)/shard_map/ppermute | solution.py:27
  14.1 25.9 %copy-start.1 = (bf16[512,4096]{1,0:T(8,128)(2,1)S(1)}, bf16[512,4096]{1,0:T(8,128)(2,1)}, u32[]{:S(2)}) copy-start(bf16[512,4096]{1,0:T(8,128)(2,1)} %slab_ref.3) | copy-start | bytes 12582916
  14.1 6.7 %collective-permute-start.11 = (bf16[128,256]{1,0:T(8,128)(2,1)S(1)}, bf16[128,256]{1,0:T(8,128)(2,1)S(1)}, u32[]{:S(2)}, u32[]{:S(2)}) collective-permute-start(bf16[128,256]{1,0:T(8,128)(2,1)S(1)} %select_convert_fusion.5), channel_id=1, source_target_pairs={{0,4},{2,6},{4,0},{6,2},{8,12},{10,14},{12,8},{14,10},{1,5},{3,7},... | collective-permute-start | bytes 196616 | tf_op jit(solution)/shard_map/ppermute | solution.py:27
  16.0 5.8 %collective-permute-start.6 = (bf16[128,256]{1,0:T(8,128)(2,1)S(1)}, bf16[128,256]{1,0:T(8,128)(2,1)S(1)}, u32[]{:S(2)}, u32[]{:S(2)}) collective-permute-start(bf16[128,256]{1,0:T(8,128)(2,1)S(1)} %select_convert_fusion.6), channel_id=1, source_target_pairs={{0,2},{2,0},{4,6},{6,4},{8,10},{10,8},{12,14},{14,12},{1,3},{3,1},... | collective-permute-start | bytes 196616 | tf_op jit(solution)/shard_map/ppermute | solution.py:27
  16.7 7.3 %collective-permute-start.1 = (bf16[128,256]{1,0:T(8,128)(2,1)S(1)}, bf16[128,256]{1,0:T(8,128)(2,1)S(1)}, u32[]{:S(2)}, u32[]{:S(2)}) collective-permute-start(bf16[128,256]{1,0:T(8,128)(2,1)S(1)} %select_convert_fusion.7), channel_id=1, source_target_pairs={{0,4},{2,6},{4,0},{6,2},{8,12},{10,14},{12,8},{14,10},{1,5},{3,7},... | collective-permute-start | bytes 196616 | tf_op jit(solution)/shard_map/ppermute | solution.py:27
  18.2 8.8 %collective-permute-start.17 = (bf16[128,256]{1,0:T(8,128)(2,1)S(1)}, bf16[128,256]{1,0:T(8,128)(2,1)S(1)}, u32[]{:S(2)}, u32[]{:S(2)}) collective-permute-start(bf16[128,256]{1,0:T(8,128)(2,1)S(1)} %fusion.25), channel_id=1, source_target_pairs={{0,8},{2,10},{4,12},{6,14},{8,0},{10,2},{12,4},{14,6},{1,9},{3,11}... | collective-permute-start | bytes 196616 | tf_op jit(solution)/shard_map/ppermute | solution.py:27
  20.9 9.1 %collective-permute-start.12 = (bf16[128,256]{1,0:T(8,128)(2,1)S(1)}, bf16[128,256]{1,0:T(8,128)(2,1)S(1)}, u32[]{:S(2)}, u32[]{:S(2)}) collective-permute-start(bf16[128,256]{1,0:T(8,128)(2,1)S(1)} %fusion.24), channel_id=1, source_target_pairs={{0,8},{2,10},{4,12},{6,14},{8,0},{10,2},{12,4},{14,6},{1,9},{3,11}... | collective-permute-start | bytes 196616 | tf_op jit(solution)/shard_map/ppermute | solution.py:27
  21.8 9.3 %collective-permute-start.7 = (bf16[128,256]{1,0:T(8,128)(2,1)S(1)}, bf16[128,256]{1,0:T(8,128)(2,1)S(1)}, u32[]{:S(2)}, u32[]{:S(2)}) collective-permute-start(bf16[128,256]{1,0:T(8,128)(2,1)S(1)} %fusion.23), channel_id=1, source_target_pairs={{0,8},{2,10},{4,12},{6,14},{8,0},{10,2},{12,4},{14,6},{1,9},{3,11}... | collective-permute-start | bytes 196616 | tf_op jit(solution)/shard_map/ppermute | solution.py:27
  24.0 8.3 %collective-permute-start.2 = (bf16[128,256]{1,0:T(8,128)(2,1)S(1)}, bf16[128,256]{1,0:T(8,128)(2,1)S(1)}, u32[]{:S(2)}, u32[]{:S(2)}) collective-permute-start(bf16[128,256]{1,0:T(8,128)(2,1)S(1)} %fusion.22), channel_id=1, source_target_pairs={{0,8},{2,10},{4,12},{6,14},{8,0},{10,2},{12,4},{14,6},{1,9},{3,11}... | collective-permute-start | bytes 196616 | tf_op jit(solution)/shard_map/ppermute | solution.py:27
  27.1 6.4 %collective-permute-start.18 = (bf16[128,256]{1,0:T(8,128)(2,1)S(1)}, bf16[128,256]{1,0:T(8,128)(2,1)S(1)}, u32[]{:S(2)}, u32[]{:S(2)}) collective-permute-start(bf16[128,256]{1,0:T(8,128)(2,1)S(1)} %multiply_convert_fusion), channel_id=1, source_target_pairs={{0,2},{2,0},{4,6},{6,4},{8,10},{10,8},{12,14},{14,12},{1,3},{3,1},... | collective-permute-start | bytes 196616 | tf_op jit(solution)/shard_map/ppermute | solution.py:27
  30.0 5.0 %collective-permute-start.13 = (bf16[128,256]{1,0:T(8,128)(2,1)S(1)}, bf16[128,256]{1,0:T(8,128)(2,1)S(1)}, u32[]{:S(2)}, u32[]{:S(2)}) collective-permute-start(bf16[128,256]{1,0:T(8,128)(2,1)S(1)} %multiply_convert_fusion.1), channel_id=1, source_target_pairs={{0,4},{2,6},{4,0},{6,2},{8,12},{10,14},{12,8},{14,10},{1,5},{3,7},... | collective-permute-start | bytes 196616 | tf_op jit(solution)/shard_map/ppermute | solution.py:27
  31.1 5.2 %collective-permute-start.8 = (bf16[128,256]{1,0:T(8,128)(2,1)S(1)}, bf16[128,256]{1,0:T(8,128)(2,1)S(1)}, u32[]{:S(2)}, u32[]{:S(2)}) collective-permute-start(bf16[128,256]{1,0:T(8,128)(2,1)S(1)} %multiply_convert_fusion.2), channel_id=1, source_target_pairs={{0,2},{2,0},{4,6},{6,4},{8,10},{10,8},{12,14},{14,12},{1,3},{3,1},... | collective-permute-start | bytes 196616 | tf_op jit(solution)/shard_map/ppermute | solution.py:27
  32.3 5.1 %collective-permute-start.3 = (bf16[128,256]{1,0:T(8,128)(2,1)S(1)}, bf16[128,256]{1,0:T(8,128)(2,1)S(1)}, u32[]{:S(2)}, u32[]{:S(2)}) collective-permute-start(bf16[128,256]{1,0:T(8,128)(2,1)S(1)} %multiply_convert_fusion.3), channel_id=1, source_target_pairs={{0,4},{2,6},{4,0},{6,2},{8,12},{10,14},{12,8},{14,10},{1,5},{3,7},... | collective-permute-start | bytes 196616 | tf_op jit(solution)/shard_map/ppermute | solution.py:27
  33.5 6.4 %collective-permute-start.19 = (bf16[128,512]{1,0:T(8,128)(2,1)S(1)}, bf16[128,512]{1,0:T(8,128)(2,1)S(1)}, u32[]{:S(2)}, u32[]{:S(2)}) collective-permute-start(bf16[128,512]{1,0:T(8,128)(2,1)S(1)} %pad_maximum_fusion.4), channel_id=1, source_target_pairs={{0,4},{2,6},{4,0},{6,2},{8,12},{10,14},{12,8},{14,10},{1,5},{3,7},... | collective-permute-start | bytes 393224 | tf_op jit(solution)/shard_map/ppermute | solution.py:27
  35.1 5.6 %collective-permute-start.14 = (bf16[128,512]{1,0:T(8,128)(2,1)S(1)}, bf16[128,512]{1,0:T(8,128)(2,1)S(1)}, u32[]{:S(2)}, u32[]{:S(2)}) collective-permute-start(bf16[128,512]{1,0:T(8,128)(2,1)S(1)} %pad_maximum_fusion.3), channel_id=1, source_target_pairs={{0,2},{2,0},{4,6},{6,4},{8,10},{10,8},{12,14},{14,12},{1,3},{3,1},... | collective-permute-start | bytes 393224 | tf_op jit(solution)/shard_map/ppermute | solution.py:27
  36.3 5.0 %collective-permute-start.9 = (bf16[128,512]{1,0:T(8,128)(2,1)S(1)}, bf16[128,512]{1,0:T(8,128)(2,1)S(1)}, u32[]{:S(2)}, u32[]{:S(2)}) collective-permute-start(bf16[128,512]{1,0:T(8,128)(2,1)S(1)} %pad_maximum_fusion.2), channel_id=1, source_target_pairs={{0,4},{2,6},{4,0},{6,2},{8,12},{10,14},{12,8},{14,10},{1,5},{3,7},... | collective-permute-start | bytes 393224 | tf_op jit(solution)/shard_map/ppermute | solution.py:27
  37.5 5.0 %collective-permute-start.4 = (bf16[128,512]{1,0:T(8,128)(2,1)S(1)}, bf16[128,512]{1,0:T(8,128)(2,1)S(1)}, u32[]{:S(2)}, u32[]{:S(2)}) collective-permute-start(bf16[128,512]{1,0:T(8,128)(2,1)S(1)} %pad_maximum_fusion.1), channel_id=1, source_target_pairs={{0,2},{2,0},{4,6},{6,4},{8,10},{10,8},{12,14},{14,12},{1,3},{3,1},... | collective-permute-start | bytes 393224 | tf_op jit(solution)/shard_map/ppermute | solution.py:27
  43.0 1.6 %collective-permute-start.20 = (f32[512,128]{1,0:T(8,128)S(1)}, f32[512,128]{1,0:T(8,128)S(1)}, u32[]{:S(2)}, u32[]{:S(2)}) collective-permute-start(f32[512,128]{1,0:T(8,128)S(1)} %fusion.2.mine_ref), channel_id=1, source_target_pairs={{0,1},{1,0},{2,3},{3,2},{4,5},{5,4},{6,7},{7,6},{8,9},{9,8},{10,11... | collective-permute-start | bytes 786440 | tf_op jit(solution)/shard_map/ppermute | solution.py:27
  45.1 6.0 %collective-permute-start.23 = (f32[72,128]{1,0:T(8,128)S(1)}, f32[72,128]{1,0:T(8,128)S(1)}, u32[]{:S(2)}, u32[]{:S(2)}) collective-permute-start(f32[72,128]{1,0:T(8,128)S(1)} %make_gram.1), channel_id=1, source_target_pairs={{0,8},{1,13},{2,10},{3,15},{4,12},{5,9},{6,14},{7,11},{8,0},{9,5},... | collective-permute-start | bytes 110600 | tf_op jit(solution)/shard_map/ppermute | solution.py:45
  47.0 6.4 %collective-permute-start.24 = (f32[72,128]{1,0:T(8,128)S(1)}, f32[72,128]{1,0:T(8,128)S(1)}, u32[]{:S(2)}, u32[]{:S(2)}) collective-permute-start(f32[72,128]{1,0:T(8,128)S(1)} %make_gram.1), channel_id=1, source_target_pairs={{0,10},{1,15},{2,8},{3,13},{4,14},{5,11},{6,12},{7,9},{8,2},{9,7},... | collective-permute-start | bytes 110600 | tf_op jit(solution)/shard_map/ppermute | solution.py:45
  48.5 5.1 %collective-permute-start.22 = (f32[72,128]{1,0:T(8,128)S(1)}, f32[72,128]{1,0:T(8,128)S(1)}, u32[]{:S(2)}, u32[]{:S(2)}) collective-permute-start(f32[72,128]{1,0:T(8,128)S(1)} %make_gram.1), channel_id=1, source_target_pairs={{0,2},{1,7},{2,0},{3,5},{4,6},{5,3},{6,4},{7,1},{8,10},{9,15},{10,... | collective-permute-start | bytes 110600 | tf_op jit(solution)/shard_map/ppermute | solution.py:45
  49.5 4.1 %collective-permute-start.21 = (f32[72,128]{1,0:T(8,128)S(1)}, f32[72,128]{1,0:T(8,128)S(1)}, u32[]{:S(2)}, u32[]{:S(2)}) collective-permute-start(f32[72,128]{1,0:T(8,128)S(1)} %make_gram.1), channel_id=1, source_target_pairs={{1,5},{3,7},{5,1},{7,3},{9,13},{11,15},{13,9},{15,11},{17,21},{19,... | collective-permute-start | bytes 110600 | tf_op jit(solution)/shard_map/ppermute | solution.py:45
  53.7 1.4 %collective-permute-start.25 = (f32[72,128]{1,0:T(8,128)S(1)}, f32[72,128]{1,0:T(8,128)S(1)}, u32[]{:S(2)}, u32[]{:S(2)}) collective-permute-start(f32[72,128]{1,0:T(8,128)S(1)} %add_add_fusion), channel_id=1, source_target_pairs={{0,1},{1,0},{2,3},{3,2},{4,5},{5,4},{6,7},{7,6},{8,9},{9,8},{10,11... | collective-permute-start | bytes 110600 | tf_op jit(solution)/shard_map/ppermute | solution.py:27
  60.0 7.6 %collective-permute-start.32 = (bf16[1,2,16,1536]{3,2,1,0:T(8,128)(2,1)S(1)}, bf16[1,2,16,1536]{3,2,1,0:T(8,128)(2,1)S(1)}, u32[]{:S(2)}, u32[]{:S(2)}) collective-permute-start(bf16[1,2,16,1536]{3,2,1,0:T(8,128)(2,1)S(1)} %get-tuple-element.15), channel_id=1, source_target_pairs={{0,12},{2,14},{4,8},{6,10},{8,4},{10,6},{12,0},{14,2},{1,13},{3,15... | collective-permute-start | bytes 294920 | tf_op jit(solution)/shard_map/ppermute | solution.py:27
  61.9 10.7 %collective-permute-start.31 = (bf16[1,2,16,1536]{3,2,1,0:T(8,128)(2,1)S(1)}, bf16[1,2,16,1536]{3,2,1,0:T(8,128)(2,1)S(1)}, u32[]{:S(2)}, u32[]{:S(2)}) collective-permute-start(bf16[1,2,16,1536]{3,2,1,0:T(8,128)(2,1)S(1)} %get-tuple-element.16), channel_id=1, source_target_pairs={{0,8},{2,10},{4,12},{6,14},{8,0},{10,2},{12,4},{14,6},{1,9},{3,11}... | collective-permute-start | bytes 294920 | tf_op jit(solution)/shard_map/ppermute | solution.py:27
  63.2 9.3 %collective-permute-start.30 = (bf16[1,2,16,1536]{3,2,1,0:T(8,128)(2,1)S(1)}, bf16[1,2,16,1536]{3,2,1,0:T(8,128)(2,1)S(1)}, u32[]{:S(2)}, u32[]{:S(2)}) collective-permute-start(bf16[1,2,16,1536]{3,2,1,0:T(8,128)(2,1)S(1)} %get-tuple-element.14), channel_id=1, source_target_pairs={{0,4},{2,6},{4,0},{6,2},{8,12},{10,14},{12,8},{14,10},{1,5},{3,7},... | collective-permute-start | bytes 294920 | tf_op jit(solution)/shard_map/ppermute | solution.py:27
  64.5 9.3 %collective-permute-start.26 = (bf16[4,1,16,2560]{3,2,1,0:T(8,128)(2,1)S(1)}, bf16[4,1,16,2560]{3,2,1,0:T(8,128)(2,1)S(1)}, u32[]{:S(2)}, u32[]{:S(2)}) collective-permute-start(bf16[4,1,16,2560]{3,2,1,0:T(8,128)(2,1)S(1)} %dynamic-slice_convert_fusion), channel_id=1, source_target_pairs={{0,2},{2,0},{4,6},{6,4},{8,10},{10,8},{12,14},{14,12},{1,3},{3,1},... | collective-permute-start | bytes 983048 | tf_op jit(solution)/shard_map/ppermute | solution.py:27
  72.6 5.6 %collective-permute-start.33 = (bf16[1,1,16,1536]{3,2,1,0:T(8,128)(2,1)S(1)}, bf16[1,1,16,1536]{3,2,1,0:T(8,128)(2,1)S(1)}, u32[]{:S(2)}, u32[]{:S(2)}) collective-permute-start(bf16[1,1,16,1536]{3,2,1,0:T(8,128)(2,1)S(1)} %dynamic-slice_convert_fusion.7), channel_id=1, source_target_pairs={{0,2},{2,0},{4,6},{6,4},{8,10},{10,8},{12,14},{14,12},{1,3},{3,1},... | collective-permute-start | bytes 147464 | tf_op jit(solution)/shard_map/ppermute | solution.py:27
  73.8 7.2 %collective-permute-start.29 = (bf16[1,1,16,2560]{3,2,1,0:T(8,128)(2,1)S(1)}, bf16[1,1,16,2560]{3,2,1,0:T(8,128)(2,1)S(1)}, u32[]{:S(2)}, u32[]{:S(2)}) collective-permute-start(bf16[1,1,16,2560]{3,2,1,0:T(8,128)(2,1)S(1)} %get-tuple-element.18), channel_id=1, source_target_pairs={{0,12},{2,14},{4,8},{6,10},{8,4},{10,6},{12,0},{14,2},{1,13},{3,15... | collective-permute-start | bytes 245768 | tf_op jit(solution)/shard_map/ppermute | solution.py:27
  75.7 8.0 %collective-permute-start.28 = (bf16[1,1,16,2560]{3,2,1,0:T(8,128)(2,1)S(1)}, bf16[1,1,16,2560]{3,2,1,0:T(8,128)(2,1)S(1)}, u32[]{:S(2)}, u32[]{:S(2)}) collective-permute-start(bf16[1,1,16,2560]{3,2,1,0:T(8,128)(2,1)S(1)} %get-tuple-element.19), channel_id=1, source_target_pairs={{0,8},{2,10},{4,12},{6,14},{8,0},{10,2},{12,4},{14,6},{1,9},{3,11}... | collective-permute-start | bytes 245768 | tf_op jit(solution)/shard_map/ppermute | solution.py:27
  76.6 7.1 %collective-permute-start.27 = (bf16[1,1,16,2560]{3,2,1,0:T(8,128)(2,1)S(1)}, bf16[1,1,16,2560]{3,2,1,0:T(8,128)(2,1)S(1)}, u32[]{:S(2)}, u32[]{:S(2)}) collective-permute-start(bf16[1,1,16,2560]{3,2,1,0:T(8,128)(2,1)S(1)} %get-tuple-element.17), channel_id=1, source_target_pairs={{0,4},{2,6},{4,0},{6,2},{8,12},{10,14},{12,8},{14,10},{1,5},{3,7},... | collective-permute-start | bytes 245768 | tf_op jit(solution)/shard_map/ppermute | solution.py:27

commit v14 on v13

--- a/solution.py
+++ b/solution.py
@@ -55,22 +55,37 @@
     return lax.rem(lax.div(lax.axis_index(axis), stride), radix)
 
 
-def scatter_sum(value, axis, reverse):
-    levels = levels_of(lax.axis_size(axis))
-    rows = value.shape[0] // lax.axis_size(axis)
-    total = value.reshape([radix for _, radix in reversed(levels)] + [rows, value.shape[1]])
-    order = range(len(levels))
-    for level in reversed(order) if reverse else order:
-        stride, radix = levels[level]
-        dim = len(levels) - 1 - level
-        digit = digit_of(axis, stride, radix)
-        parts = total
-        total = lax.dynamic_slice_in_dim(parts, digit, 1, dim)
-        for t in range(1, radix):
-            part = lax.dynamic_slice_in_dim(parts, jnp.bitwise_xor(digit, t), 1, dim)
-            landed = swap(part.astype(jnp.bfloat16), axis, t * stride)
-            total = total + landed.astype(jnp.float32)
-    return total.reshape(rows, value.shape[1])
+def core_swap(value, bits):
+    rows, cores = lax.axis_size("row"), lax.axis_size("col")
+    pairs = [
+        (row * cores + core, (row ^ (1 << bits[core % 2])) * cores + core)
+        for row in range(rows)
+        for core in range(cores)
+    ]
+    return lax.ppermute(value, ("row", "col"), pairs)
+
+
+def core_upper(bits):
+    odd = lax.rem(lax.axis_index("col"), 2) == 1
+    weight = jnp.where(odd, 1 << bits[1], 1 << bits[0])
+    return jnp.bitwise_and(lax.axis_index("row"), weight) != 0
+
+
+def scatter_sum(value):
+    n = lax.axis_size("row")
+    bits = (n - 1).bit_length()
+    rows, cols = value.shape[0] // n, value.shape[1]
+    odd = lax.rem(lax.axis_index("col"), 2) == 1
+    view = value.reshape(n // 4, 2, 2, rows, cols)
+    low = jnp.where(odd, view[:, 0], view[:, :, 0])
+    high = jnp.where(odd, view[:, 1], view[:, :, 1])
+    for step in [(0, 1), (1, 0)] + [(bit, bit) for bit in range(2, bits)]:
+        upper = core_upper(step)
+        landed = core_swap(jnp.where(upper, low, high).astype(jnp.bfloat16), step)
+        total = jnp.where(upper, high, low) + landed.astype(jnp.float32)
+        total = total.reshape(-1, 2, rows, cols) if step[0] < bits - 1 else total
+        low, high = total[:, 0], total[:, -1]
+    return total.reshape(rows, cols)
 
 
 def bit_of(axis, bit):
@@ -334,12 +349,8 @@
         gram, partial_sketch, other_sketch, activations, total_cols, root_rows
     )
 
-    cut = cols_here * 5 // 8
-    pieces = [
-        scatter_sum(local_proj[:, :cut], "row", False) / total_rows,
-        scatter_sum(local_proj[:, cut:], "row", True) / total_rows,
-    ]
-    return (basis, jnp.concatenate(pieces, axis=1))
+    projection = scatter_sum(local_proj) / total_rows
+    return (basis, projection)
 
 
 def solution(mesh):

time: 84.6 us -> 93.3 us (1.10)
  waiting for transfers between devices: 27.4 us -> 43.2 us
  starting transfers between devices: 43.3 us -> 30.2 us
  other arithmetic: 1.79 us -> 5.7 us
  local copies, waits for them, and re-layouts: 1.18 us -> 3.14 us
    ppermute x0 -> x3, waiting for transfers between devices: none -> 22.1 us  [core_swap(): return lax.ppermute(value, ('row', 'col'), pairs)]
    ppermute x30 -> x22, starting transfers between devices: 38.2 us -> 24 us  [swap(): return lax.ppermute(value, axis, [(i, i ^ distance) for i in range(size)])]
    ppermute x30 -> x22, waiting for transfers between devices: 23.9 us -> 15.8 us  [swap(): return lax.ppermute(value, axis, [(i, i ^ distance) for i in range(size)])]
    unnamed x4 -> x8, local copies, waits for them, and re-layouts: 0.9 us -> 2.86 us
    ppermute x4, waiting for transfers between devices: 3.45 us -> 5.31 us  [row_sum(): terms.append(lax.ppermute(value, ('row', 'col'), pairs))]
    add x2 -> x1, other arithmetic: 0.11 us -> 1.62 us  [scatter_sum(): total = jnp.where(upper, high, low) + landed.astype(jnp.float32)]
    reshape x0 -> x1, other arithmetic: none -> 1.27 us  [scatter_sum(): total = total.reshape(-1, 2, rows, cols) if step[0] < bits - 1 else total]
    convert_element_type x0 -> x3, other arithmetic: none -> 1.16 us  [scatter_sum(): landed = core_swap(jnp.where(upper, low, high).astype(jnp.bfloat16), step)]
  transfers between devices with their start and end apart: 34 -> 29, of which waited for: 19 -> 18; matrix products, arithmetic and copies ran while one was open for 3% -> 2% of each run, Pallas kernels for 0% -> 0%
where the time goes in v14:
time: 93.3 us; the launch traced here: 93.1 us
  waiting for transfers between devices  43.2 us (46%)
  starting transfers between devices  30.2 us (32%)
  Pallas kernels  8.12 us (9%)
  other arithmetic  5.7 us (6%)
  local copies, waits for them, and re-layouts  3.14 us (3%)
  matrix products  1.75 us (2%)
  between operations  0.99 us (1%)
    ppermute x22, starting transfers between devices, swap(): return lax.ppermute(value, axis, [(i, i ^ distance) for i in range(size)])  24 us
    ppermute x3, waiting for transfers between devices, core_swap(): return lax.ppermute(value, ('row', 'col'), pairs)  22.1 us
    ppermute x22, waiting for transfers between devices, swap(): return lax.ppermute(value, axis, [(i, i ^ distance) for i in range(size)])  15.8 us
    ppermute x4, waiting for transfers between devices, row_sum(): terms.append(lax.ppermute(value, ('row', 'col'), pairs))  5.31 us
    ppermute x4, starting transfers between devices, row_sum(): terms.append(lax.ppermute(value, ('row', 'col'), pairs))  5.12 us
    pallas_call x1, Pallas kernels, make_basis(): pl.pallas_call(functools.partial(basis_kernel, total_cols, root_rows), ou...  4.63 us
    pallas_call x1, Pallas kernels, first_product(): pl.pallas_call(sketch_kernel, out_shape=[jax.ShapeDtypeStruct((width, col...  2.99 us
    unnamed x8, local copies, waits for them, and re-layouts  2.86 us
  transfers between devices with their start and end apart: 29, of which 18 were waited for; matrix products, arithmetic and copies ran while one was open for 2% of the time, Pallas kernels for 0%

profile of v14, /device:TPU:0, one launch (start us, length us, event | category | flops | bytes accessed | tf_op | source)
XLA Modules:
  0.0 93.1 jit_solution(11603163210031353710)
XLA Ops:
  0.6 0.9 copy-done
  1.5 3.0 %first_product.1 = (f32[128,1024]{1,0:T(8,128)S(1)}, f32[128,1024]{1,0:T(8,128)S(1)}, f32[128,1024]{1,0:T(8,128)S(1)}, f32[128,1024]{1,0:T(8,128)S(1)}) custom-call(bf16[512,128]{1,0:T(8,128)(2,1)S(1)} %copy-done, bf16[512,4096]{1,0:T(8,128)(2,1)} %slab_ref.3), custom_call_target="tpu_custom_call" | custom-call | flops 536870912 | bytes 4194304 | tf_op jit(solution)/shard_map/first_product/pallas_call | solution.py:148
  4.6 3.0 %collective-permute-start = (bf16[128,512]{1,0:T(8,128)(2,1)S(1)}, bf16[128,512]{1,0:T(8,128)(2,1)S(1)}, u32[]{:S(2)}, u32[]{:S(2)}) collective-permute-start(bf16[128,512]{1,0:T(8,128)(2,1)S(1)} %select_convert_fusion.6), channel_id=1, source_target_pairs={{0,2},{2,0},{4,6},{6,4},{8,10},{10,8},{12,14},{14,12},{1,3},{3,1},... | collective-permute-start | bytes 393224 | tf_op jit(solution)/shard_map/ppermute | solution.py:27
  7.6 1.6 %collective-permute-start.5 = (bf16[128,512]{1,0:T(8,128)(2,1)S(1)}, bf16[128,512]{1,0:T(8,128)(2,1)S(1)}, u32[]{:S(2)}, u32[]{:S(2)}) collective-permute-start(bf16[128,512]{1,0:T(8,128)(2,1)S(1)} %select_convert_fusion.5), channel_id=1, source_target_pairs={{0,4},{2,6},{4,0},{6,2},{8,12},{10,14},{12,8},{14,10},{1,5},{3,7},... | collective-permute-start | bytes 393224 | tf_op jit(solution)/shard_map/ppermute | solution.py:27
  9.3 0.6 collective-permute-start.10
  10.0 1.4 %collective-permute-done = bf16[128,512]{1,0:T(8,128)(2,1)S(1)} collective-permute-done((bf16[128,512]{1,0:T(8,128)(2,1)S(1)}, bf16[128,512]{1,0:T(8,128)(2,1)S(1)}, u32[]{:S(2)}, u32[]{:S(2)}) %collective-permute-start) | collective-permute-done | bytes 131104 | tf_op jit(solution)/shard_map/ppermute | solution.py:27
  11.5 2.7 %collective-permute-start.1 = (bf16[128,256]{1,0:T(8,128)(2,1)S(1)}, bf16[128,256]{1,0:T(8,128)(2,1)S(1)}, u32[]{:S(2)}, u32[]{:S(2)}) collective-permute-start(bf16[128,256]{1,0:T(8,128)(2,1)S(1)} %select_convert_fusion.10), channel_id=1, source_target_pairs={{0,4},{2,6},{4,0},{6,2},{8,12},{10,14},{12,8},{14,10},{1,5},{3,7},... | collective-permute-start | bytes 196616 | tf_op jit(solution)/shard_map/ppermute | solution.py:27
  14.3 1.6 %collective-permute-start.6 = (bf16[128,256]{1,0:T(8,128)(2,1)S(1)}, bf16[128,256]{1,0:T(8,128)(2,1)S(1)}, u32[]{:S(2)}, u32[]{:S(2)}) collective-permute-start(bf16[128,256]{1,0:T(8,128)(2,1)S(1)} %select_convert_fusion.9), channel_id=1, source_target_pairs={{0,2},{2,0},{4,6},{6,4},{8,10},{10,8},{12,14},{14,12},{1,3},{3,1},... | collective-permute-start | bytes 196616 | tf_op jit(solution)/shard_map/ppermute | solution.py:27
  16.5 1.7 %collective-permute-start.16 = (bf16[128,256]{1,0:T(8,128)(2,1)S(1)}, bf16[128,256]{1,0:T(8,128)(2,1)S(1)}, u32[]{:S(2)}, u32[]{:S(2)}) collective-permute-start(bf16[128,256]{1,0:T(8,128)(2,1)S(1)} %select_convert_fusion.7), channel_id=1, source_target_pairs={{0,2},{2,0},{4,6},{6,4},{8,10},{10,8},{12,14},{14,12},{1,3},{3,1},... | collective-permute-start | bytes 196616 | tf_op jit(solution)/shard_map/ppermute | solution.py:27
  18.2 2.7 %collective-permute-start.2 = (bf16[128,256]{1,0:T(8,128)(2,1)S(1)}, bf16[128,256]{1,0:T(8,128)(2,1)S(1)}, u32[]{:S(2)}, u32[]{:S(2)}) collective-permute-start(bf16[128,256]{1,0:T(8,128)(2,1)S(1)} %fusion.29), channel_id=1, source_target_pairs={{0,8},{2,10},{4,12},{6,14},{8,0},{10,2},{12,4},{14,6},{1,9},{3,11}... | collective-permute-start | bytes 196616 | tf_op jit(solution)/shard_map/ppermute | solution.py:27
  20.9 0.5 collective-permute-start.7
  21.4 2.6 %collective-permute-start.12 = (bf16[128,256]{1,0:T(8,128)(2,1)S(1)}, bf16[128,256]{1,0:T(8,128)(2,1)S(1)}, u32[]{:S(2)}, u32[]{:S(2)}) collective-permute-start(bf16[128,256]{1,0:T(8,128)(2,1)S(1)} %fusion.31), channel_id=1, source_target_pairs={{0,8},{2,10},{4,12},{6,14},{8,0},{10,2},{12,4},{14,6},{1,9},{3,11}... | collective-permute-start | bytes 196616 | tf_op jit(solution)/shard_map/ppermute | solution.py:27
  24.0 0.5 collective-permute-start.17
  24.5 3.7 %collective-permute-done.2 = bf16[128,256]{1,0:T(8,128)(2,1)S(1)} collective-permute-done((bf16[128,256]{1,0:T(8,128)(2,1)S(1)}, bf16[128,256]{1,0:T(8,128)(2,1)S(1)}, u32[]{:S(2)}, u32[]{:S(2)}) %collective-permute-start.2) | collective-permute-done | bytes 65568 | tf_op jit(solution)/shard_map/ppermute | solution.py:27
  28.5 1.8 %collective-permute-done.7 = bf16[128,256]{1,0:T(8,128)(2,1)S(1)} collective-permute-done((bf16[128,256]{1,0:T(8,128)(2,1)S(1)}, bf16[128,256]{1,0:T(8,128)(2,1)S(1)}, u32[]{:S(2)}, u32[]{:S(2)}) %collective-permute-start.7) | collective-permute-done | bytes 65568 | tf_op jit(solution)/shard_map/ppermute | solution.py:27
  30.4 0.6 collective-permute-done.12
  31.3 0.5 collective-permute-done.17
  31.8 0.8 collective-permute-start.18
  32.7 0.5 collective-permute-done.3
  33.2 0.9 collective-permute-start.4
  34.0 1.3 %collective-permute-done.8 = bf16[128,256]{1,0:T(8,128)(2,1)S(1)} collective-permute-done((bf16[128,256]{1,0:T(8,128)(2,1)S(1)}, bf16[128,256]{1,0:T(8,128)(2,1)S(1)}, u32[]{:S(2)}, u32[]{:S(2)}) %collective-permute-start.8) | collective-permute-done | bytes 65568 | tf_op jit(solution)/shard_map/ppermute | solution.py:27
  35.5 0.5 collective-permute-done.13
  36.0 1.4 %collective-permute-start.14 = (bf16[128,512]{1,0:T(8,128)(2,1)S(1)}, bf16[128,512]{1,0:T(8,128)(2,1)S(1)}, u32[]{:S(2)}, u32[]{:S(2)}) collective-permute-start(bf16[128,512]{1,0:T(8,128)(2,1)S(1)} %pad_maximum_fusion.2), channel_id=1, source_target_pairs={{0,2},{2,0},{4,6},{6,4},{8,10},{10,8},{12,14},{14,12},{1,3},{3,1},... | collective-permute-start | bytes 393224 | tf_op jit(solution)/shard_map/ppermute | solution.py:27
  37.4 0.9 collective-permute-start.19
  38.3 2.1 %collective-permute-done.9 = bf16[128,512]{1,0:T(8,128)(2,1)S(1)} collective-permute-done((bf16[128,512]{1,0:T(8,128)(2,1)S(1)}, bf16[128,512]{1,0:T(8,128)(2,1)S(1)}, u32[]{:S(2)}, u32[]{:S(2)}) %collective-permute-start.9) | collective-permute-done | bytes 131104 | tf_op jit(solution)/shard_map/ppermute | solution.py:27
  41.5 0.9 collective-permute-done.19
  43.0 0.4 fusion.2.mine_ref
  43.5 1.5 %collective-permute-done.20.other_ref = f32[512,128]{1,0:T(8,128)S(1)} collective-permute-done((f32[512,128]{1,0:T(8,128)S(1)}, f32[512,128]{1,0:T(8,128)S(1)}, u32[]{:S(2)}, u32[]{:S(2)}) %collective-permute-start.20) | collective-permute-done | bytes 262176 | tf_op jit(solution)/shard_map/ppermute | solution.py:27
  45.0 0.5 make_gram.1
  45.5 0.7 collective-permute-start.21
  46.2 0.8 collective-permute-start.22
  47.0 2.3 %collective-permute-start.23 = (f32[72,128]{1,0:T(8,128)S(1)}, f32[72,128]{1,0:T(8,128)S(1)}, u32[]{:S(2)}, u32[]{:S(2)}) collective-permute-start(f32[72,128]{1,0:T(8,128)S(1)} %make_gram.1), channel_id=1, source_target_pairs={{0,8},{1,13},{2,10},{3,15},{4,12},{5,9},{6,14},{7,11},{8,0},{9,5},... | collective-permute-start | bytes 110600 | tf_op jit(solution)/shard_map/ppermute | solution.py:45
  49.3 1.4 %collective-permute-start.24 = (f32[72,128]{1,0:T(8,128)S(1)}, f32[72,128]{1,0:T(8,128)S(1)}, u32[]{:S(2)}, u32[]{:S(2)}) collective-permute-start(f32[72,128]{1,0:T(8,128)S(1)} %make_gram.1), channel_id=1, source_target_pairs={{0,10},{1,15},{2,8},{3,13},{4,14},{5,11},{6,12},{7,9},{8,2},{9,7},... | collective-permute-start | bytes 110600 | tf_op jit(solution)/shard_map/ppermute | solution.py:45
  50.7 1.2 %collective-permute-done.23 = f32[72,128]{1,0:T(8,128)S(1)} collective-permute-done((f32[72,128]{1,0:T(8,128)S(1)}, f32[72,128]{1,0:T(8,128)S(1)}, u32[]{:S(2)}, u32[]{:S(2)}) %collective-permute-start.23) | collective-permute-done | bytes 36896 | tf_op jit(solution)/shard_map/ppermute | solution.py:45
  51.9 4.1 %collective-permute-done.24 = f32[72,128]{1,0:T(8,128)S(1)} collective-permute-done((f32[72,128]{1,0:T(8,128)S(1)}, f32[72,128]{1,0:T(8,128)S(1)}, u32[]{:S(2)}, u32[]{:S(2)}) %collective-permute-start.24) | collective-permute-done | bytes 36896 | tf_op jit(solution)/shard_map/ppermute | solution.py:45
  56.0 1.3 %collective-permute-start.25 = (f32[72,128]{1,0:T(8,128)S(1)}, f32[72,128]{1,0:T(8,128)S(1)}, u32[]{:S(2)}, u32[]{:S(2)}) collective-permute-start(f32[72,128]{1,0:T(8,128)S(1)} %add_add_fusion), channel_id=1, source_target_pairs={{0,1},{1,0},{2,3},{3,2},{4,5},{5,4},{6,7},{7,6},{8,9},{9,8},{10,11... | collective-permute-start | bytes 110600 | tf_op jit(solution)/shard_map/ppermute | solution.py:27
  57.3 0.9 collective-permute-done.25
  58.2 4.6 %make_basis.1 = (f32[512,128]{1,0:T(8,128)}, f32[128,4096]{1,0:T(8,128)S(1)}) custom-call(f32[72,128]{1,0:T(8,128)S(1)} %add.89.gram_ref, f32[512,128]{1,0:T(8,128)S(1)} %fusion.2.mine_ref, f32[512,128]{1,0:T(8,128)S(1)} %collective-permute-done.20.other_ref, bf16[512,4096]{1,0:T(8,128)(2,1)} %slab_ref.3), custom_call_target="tpu_custom_call" | custom-call | tf_op jit(solution)/shard_map/make_basis/pallas_call | solution.py:305
  63.1 1.0 %copy-done.2 = f32[2,2,1,16,4096]{4,3,2,1,0:T(8,128)} copy-done((f32[2,2,1,16,4096]{4,3,2,1,0:T(8,128)}, f32[2,2,1,16,4096]{4,3,2,1,0:T(8,128)S(1)}, u32[]{:S(2)}) %copy-start.2) | copy-done | bytes 1048600
  64.1 1.1 %select_convert_fusion = bf16[2,2,16,4096]{3,2,0,1:T(8,128)(2,1)} fusion(pred[]{:T(512)S(6)} %ne.11, f32[2,2,1,16,4096]{4,3,2,1,0:T(8,128)S(1)} %get-tuple-element.17, f32[2,1,2,16,4096]{4,3,2,1,0:T(8,128)S(1)} %get-tuple-element.15, pred[]{:T(512)S(6)} %eq.11, f32[2,2,1,16,4096]{4,3,2,1,0:T(8,128)S(1)} %get-tuple-element.16, ...), kind=kLoop, calls=%fused_computation.11 | loop fusion | flops 786432 | bytes 4718594 | tf_op jit(solution)/shard_map/convert_element_type | solution.py:84
  65.2 0.9 %collective-permute-start.26 = (bf16[2,2,16,4096]{3,2,0,1:T(8,128)(2,1)}, bf16[2,2,16,4096]{3,2,0,1:T(8,128)(2,1)}, u32[]{:S(2)}, u32[]{:S(2)}) collective-permute-start(bf16[2,2,16,4096]{3,2,0,1:T(8,128)(2,1)} %select_convert_fusion), channel_id=1, source_target_pairs={{0,2},{1,5},{2,0},{3,7},{4,6},{5,1},{6,4},{7,3},{8,10},{9,13},{10,... | collective-permute-start | bytes 1572872 | tf_op jit(solution)/shard_map/ppermute | solution.py:65
  66.1 8.6 %collective-permute-done.26 = bf16[2,2,16,4096]{3,2,0,1:T(8,128)(2,1)} collective-permute-done((bf16[2,2,16,4096]{3,2,0,1:T(8,128)(2,1)}, bf16[2,2,16,4096]{3,2,0,1:T(8,128)(2,1)}, u32[]{:S(2)}, u32[]{:S(2)}) %collective-permute-start.26) | collective-permute-done | bytes 524320 | tf_op jit(solution)/shard_map/ppermute | solution.py:65
  74.7 1.6 %convert_add_fusion = f32[2,2,16,4096]{3,2,0,1:T(8,128)S(1)} fusion(bf16[2,2,16,4096]{3,2,0,1:T(8,128)(2,1)} %collective-permute-done.26, pred[]{:T(512)S(6)} %ne.11, f32[2,2,1,16,4096]{4,3,2,1,0:T(8,128)} %copy-done.2, f32[2,1,2,16,4096]{4,3,2,1,0:T(8,128)S(1)} %get-tuple-element.15, pred[]{:T(512)S(6)} %eq.11, ...), kind=kLoop, calls=%fused_computation.10 | loop fusion | flops 1310720 | bytes 5767170 | tf_op jit(solution)/shard_map/add | solution.py:85
  76.3 1.0 %copy-done.3 = f32[2,2,16,4096]{3,2,0,1:T(8,128)} copy-done((f32[2,2,16,4096]{3,2,0,1:T(8,128)}, f32[2,2,16,4096]{3,2,0,1:T(8,128)S(1)}, u32[]{:S(2)}) %copy-start.3) | copy-done | bytes 1048600
  77.4 6.4 %collective-permute-done.27 = bf16[2,16,4096]{2,1,0:T(8,128)(2,1)S(1)} collective-permute-done((bf16[2,16,4096]{2,1,0:T(8,128)(2,1)S(1)}, bf16[2,16,4096]{2,1,0:T(8,128)(2,1)S(1)}, u32[]{:S(2)}, u32[]{:S(2)}) %collective-permute-start.27) | collective-permute-done | bytes 262176 | tf_op jit(solution)/shard_map/ppermute | solution.py:65
  83.8 1.3 %fusion.12 = f32[1,2,16,4096]{3,2,1,0:T(8,128)S(1)} fusion(bf16[2,16,4096]{2,1,0:T(8,128)(2,1)S(1)} %collective-permute-done.27, f32[2,2,16,4096]{3,2,0,1:T(8,128)} %copy-done.3, pred[]{:T(512)S(6)} %ne.10), kind=kLoop, calls=%fused_computation.20 | loop fusion | flops 393216 | bytes 1835009 | tf_op jit(solution)/shard_map/reshape | solution.py:86
  85.2 7.2 %collective-permute-done.28 = bf16[1,16,4096]{2,1,0:T(8,128)(2,1)S(1)} collective-permute-done((bf16[1,16,4096]{2,1,0:T(8,128)(2,1)S(1)}, bf16[1,16,4096]{2,1,0:T(8,128)(2,1)S(1)}, u32[]{:S(2)}, u32[]{:S(2)}) %collective-permute-start.28) | collective-permute-done | bytes 131104 | tf_op jit(solution)/shard_map/ppermute | solution.py:65
  92.3 0.8 fusion.27
  (67 shorter events, 4.2 us)
Async XLA Ops:
  0.6 0.9 copy-start
  4.6 6.8 %collective-permute-start = (bf16[128,512]{1,0:T(8,128)(2,1)S(1)}, bf16[128,512]{1,0:T(8,128)(2,1)S(1)}, u32[]{:S(2)}, u32[]{:S(2)}) collective-permute-start(bf16[128,512]{1,0:T(8,128)(2,1)S(1)} %select_convert_fusion.6), channel_id=1, source_target_pairs={{0,2},{2,0},{4,6},{6,4},{8,10},{10,8},{12,14},{14,12},{1,3},{3,1},... | collective-permute-start | bytes 393224 | tf_op jit(solution)/shard_map/ppermute | solution.py:27
  7.6 6.6 %collective-permute-start.5 = (bf16[128,512]{1,0:T(8,128)(2,1)S(1)}, bf16[128,512]{1,0:T(8,128)(2,1)S(1)}, u32[]{:S(2)}, u32[]{:S(2)}) collective-permute-start(bf16[128,512]{1,0:T(8,128)(2,1)S(1)} %select_convert_fusion.5), channel_id=1, source_target_pairs={{0,4},{2,6},{4,0},{6,2},{8,12},{10,14},{12,8},{14,10},{1,5},{3,7},... | collective-permute-start | bytes 393224 | tf_op jit(solution)/shard_map/ppermute | solution.py:27
  9.3 6.6 %collective-permute-start.10 = (bf16[128,512]{1,0:T(8,128)(2,1)S(1)}, bf16[128,512]{1,0:T(8,128)(2,1)S(1)}, u32[]{:S(2)}, u32[]{:S(2)}) collective-permute-start(bf16[128,512]{1,0:T(8,128)(2,1)S(1)} %select_convert_fusion.4), channel_id=1, source_target_pairs={{0,2},{2,0},{4,6},{6,4},{8,10},{10,8},{12,14},{14,12},{1,3},{3,1},... | collective-permute-start | bytes 393224 | tf_op jit(solution)/shard_map/ppermute | solution.py:27
  9.9 6.5 %collective-permute-start.15 = (bf16[128,512]{1,0:T(8,128)(2,1)S(1)}, bf16[128,512]{1,0:T(8,128)(2,1)S(1)}, u32[]{:S(2)}, u32[]{:S(2)}) collective-permute-start(bf16[128,512]{1,0:T(8,128)(2,1)S(1)} %select_convert_fusion.3), channel_id=1, source_target_pairs={{0,4},{2,6},{4,0},{6,2},{8,12},{10,14},{12,8},{14,10},{1,5},{3,7},... | collective-permute-start | bytes 393224 | tf_op jit(solution)/shard_map/ppermute | solution.py:27
  11.5 6.7 %collective-permute-start.1 = (bf16[128,256]{1,0:T(8,128)(2,1)S(1)}, bf16[128,256]{1,0:T(8,128)(2,1)S(1)}, u32[]{:S(2)}, u32[]{:S(2)}) collective-permute-start(bf16[128,256]{1,0:T(8,128)(2,1)S(1)} %select_convert_fusion.10), channel_id=1, source_target_pairs={{0,4},{2,6},{4,0},{6,2},{8,12},{10,14},{12,8},{14,10},{1,5},{3,7},... | collective-permute-start | bytes 196616 | tf_op jit(solution)/shard_map/ppermute | solution.py:27
  14.3 26.2 %copy-start.1 = (bf16[512,4096]{1,0:T(8,128)(2,1)S(1)}, bf16[512,4096]{1,0:T(8,128)(2,1)}, u32[]{:S(2)}) copy-start(bf16[512,4096]{1,0:T(8,128)(2,1)} %slab_ref.3) | copy-start | bytes 12582916
  14.3 6.6 %collective-permute-start.6 = (bf16[128,256]{1,0:T(8,128)(2,1)S(1)}, bf16[128,256]{1,0:T(8,128)(2,1)S(1)}, u32[]{:S(2)}, u32[]{:S(2)}) collective-permute-start(bf16[128,256]{1,0:T(8,128)(2,1)S(1)} %select_convert_fusion.9), channel_id=1, source_target_pairs={{0,2},{2,0},{4,6},{6,4},{8,10},{10,8},{12,14},{14,12},{1,3},{3,1},... | collective-permute-start | bytes 196616 | tf_op jit(solution)/shard_map/ppermute | solution.py:27
  15.9 5.4 %collective-permute-start.11 = (bf16[128,256]{1,0:T(8,128)(2,1)S(1)}, bf16[128,256]{1,0:T(8,128)(2,1)S(1)}, u32[]{:S(2)}, u32[]{:S(2)}) collective-permute-start(bf16[128,256]{1,0:T(8,128)(2,1)S(1)} %select_convert_fusion.8), channel_id=1, source_target_pairs={{0,4},{2,6},{4,0},{6,2},{8,12},{10,14},{12,8},{14,10},{1,5},{3,7},... | collective-permute-start | bytes 196616 | tf_op jit(solution)/shard_map/ppermute | solution.py:27
  16.5 7.5 %collective-permute-start.16 = (bf16[128,256]{1,0:T(8,128)(2,1)S(1)}, bf16[128,256]{1,0:T(8,128)(2,1)S(1)}, u32[]{:S(2)}, u32[]{:S(2)}) collective-permute-start(bf16[128,256]{1,0:T(8,128)(2,1)S(1)} %select_convert_fusion.7), channel_id=1, source_target_pairs={{0,2},{2,0},{4,6},{6,4},{8,10},{10,8},{12,14},{14,12},{1,3},{3,1},... | collective-permute-start | bytes 196616 | tf_op jit(solution)/shard_map/ppermute | solution.py:27
  18.2 10.0 %collective-permute-start.2 = (bf16[128,256]{1,0:T(8,128)(2,1)S(1)}, bf16[128,256]{1,0:T(8,128)(2,1)S(1)}, u32[]{:S(2)}, u32[]{:S(2)}) collective-permute-start(bf16[128,256]{1,0:T(8,128)(2,1)S(1)} %fusion.29), channel_id=1, source_target_pairs={{0,8},{2,10},{4,12},{6,14},{8,0},{10,2},{12,4},{14,6},{1,9},{3,11}... | collective-permute-start | bytes 196616 | tf_op jit(solution)/shard_map/ppermute | solution.py:27
  20.9 9.4 %collective-permute-start.7 = (bf16[128,256]{1,0:T(8,128)(2,1)S(1)}, bf16[128,256]{1,0:T(8,128)(2,1)S(1)}, u32[]{:S(2)}, u32[]{:S(2)}) collective-permute-start(bf16[128,256]{1,0:T(8,128)(2,1)S(1)} %fusion.30), channel_id=1, source_target_pairs={{0,8},{2,10},{4,12},{6,14},{8,0},{10,2},{12,4},{14,6},{1,9},{3,11}... | collective-permute-start | bytes 196616 | tf_op jit(solution)/shard_map/ppermute | solution.py:27
  21.4 9.6 %collective-permute-start.12 = (bf16[128,256]{1,0:T(8,128)(2,1)S(1)}, bf16[128,256]{1,0:T(8,128)(2,1)S(1)}, u32[]{:S(2)}, u32[]{:S(2)}) collective-permute-start(bf16[128,256]{1,0:T(8,128)(2,1)S(1)} %fusion.31), channel_id=1, source_target_pairs={{0,8},{2,10},{4,12},{6,14},{8,0},{10,2},{12,4},{14,6},{1,9},{3,11}... | collective-permute-start | bytes 196616 | tf_op jit(solution)/shard_map/ppermute | solution.py:27
  24.0 7.8 %collective-permute-start.17 = (bf16[128,256]{1,0:T(8,128)(2,1)S(1)}, bf16[128,256]{1,0:T(8,128)(2,1)S(1)}, u32[]{:S(2)}, u32[]{:S(2)}) collective-permute-start(bf16[128,256]{1,0:T(8,128)(2,1)S(1)} %fusion.32), channel_id=1, source_target_pairs={{0,8},{2,10},{4,12},{6,14},{8,0},{10,2},{12,4},{14,6},{1,9},{3,11}... | collective-permute-start | bytes 196616 | tf_op jit(solution)/shard_map/ppermute | solution.py:27
  28.2 4.9 %collective-permute-start.3 = (bf16[128,256]{1,0:T(8,128)(2,1)S(1)}, bf16[128,256]{1,0:T(8,128)(2,1)S(1)}, u32[]{:S(2)}, u32[]{:S(2)}) collective-permute-start(bf16[128,256]{1,0:T(8,128)(2,1)S(1)} %multiply_convert_fusion.3), channel_id=1, source_target_pairs={{0,4},{2,6},{4,0},{6,2},{8,12},{10,14},{12,8},{14,10},{1,5},{3,7},... | collective-permute-start | bytes 196616 | tf_op jit(solution)/shard_map/ppermute | solution.py:27
  30.3 5.0 %collective-permute-start.8 = (bf16[128,256]{1,0:T(8,128)(2,1)S(1)}, bf16[128,256]{1,0:T(8,128)(2,1)S(1)}, u32[]{:S(2)}, u32[]{:S(2)}) collective-permute-start(bf16[128,256]{1,0:T(8,128)(2,1)S(1)} %multiply_convert_fusion.2), channel_id=1, source_target_pairs={{0,2},{2,0},{4,6},{6,4},{8,10},{10,8},{12,14},{14,12},{1,3},{3,1},... | collective-permute-start | bytes 196616 | tf_op jit(solution)/shard_map/ppermute | solution.py:27
  31.1 4.9 %collective-permute-start.13 = (bf16[128,256]{1,0:T(8,128)(2,1)S(1)}, bf16[128,256]{1,0:T(8,128)(2,1)S(1)}, u32[]{:S(2)}, u32[]{:S(2)}) collective-permute-start(bf16[128,256]{1,0:T(8,128)(2,1)S(1)} %multiply_convert_fusion.1), channel_id=1, source_target_pairs={{0,4},{2,6},{4,0},{6,2},{8,12},{10,14},{12,8},{14,10},{1,5},{3,7},... | collective-permute-start | bytes 196616 | tf_op jit(solution)/shard_map/ppermute | solution.py:27
  31.8 5.5 %collective-permute-start.18 = (bf16[128,256]{1,0:T(8,128)(2,1)S(1)}, bf16[128,256]{1,0:T(8,128)(2,1)S(1)}, u32[]{:S(2)}, u32[]{:S(2)}) collective-permute-start(bf16[128,256]{1,0:T(8,128)(2,1)S(1)} %multiply_convert_fusion), channel_id=1, source_target_pairs={{0,2},{2,0},{4,6},{6,4},{8,10},{10,8},{12,14},{14,12},{1,3},{3,1},... | collective-permute-start | bytes 196616 | tf_op jit(solution)/shard_map/ppermute | solution.py:27
  33.2 9.8 %collective-permute-start.4 = (bf16[128,512]{1,0:T(8,128)(2,1)S(1)}, bf16[128,512]{1,0:T(8,128)(2,1)S(1)}, u32[]{:S(2)}, u32[]{:S(2)}) collective-permute-start(bf16[128,512]{1,0:T(8,128)(2,1)S(1)} %pad_maximum_fusion), channel_id=1, source_target_pairs={{0,2},{2,0},{4,6},{6,4},{8,10},{10,8},{12,14},{14,12},{1,3},{3,1},... | collective-permute-start | bytes 393224 | tf_op jit(solution)/shard_map/ppermute | solution.py:27
  35.4 5.0 %collective-permute-start.9 = (bf16[128,512]{1,0:T(8,128)(2,1)S(1)}, bf16[128,512]{1,0:T(8,128)(2,1)S(1)}, u32[]{:S(2)}, u32[]{:S(2)}) collective-permute-start(bf16[128,512]{1,0:T(8,128)(2,1)S(1)} %pad_maximum_fusion.1), channel_id=1, source_target_pairs={{0,4},{2,6},{4,0},{6,2},{8,12},{10,14},{12,8},{14,10},{1,5},{3,7},... | collective-permute-start | bytes 393224 | tf_op jit(solution)/shard_map/ppermute | solution.py:27
  36.0 5.0 %collective-permute-start.14 = (bf16[128,512]{1,0:T(8,128)(2,1)S(1)}, bf16[128,512]{1,0:T(8,128)(2,1)S(1)}, u32[]{:S(2)}, u32[]{:S(2)}) collective-permute-start(bf16[128,512]{1,0:T(8,128)(2,1)S(1)} %pad_maximum_fusion.2), channel_id=1, source_target_pairs={{0,2},{2,0},{4,6},{6,4},{8,10},{10,8},{12,14},{14,12},{1,3},{3,1},... | collective-permute-start | bytes 393224 | tf_op jit(solution)/shard_map/ppermute | solution.py:27
  37.4 5.0 %collective-permute-start.19 = (bf16[128,512]{1,0:T(8,128)(2,1)S(1)}, bf16[128,512]{1,0:T(8,128)(2,1)S(1)}, u32[]{:S(2)}, u32[]{:S(2)}) collective-permute-start(bf16[128,512]{1,0:T(8,128)(2,1)S(1)} %pad_maximum_fusion.3), channel_id=1, source_target_pairs={{0,4},{2,6},{4,0},{6,2},{8,12},{10,14},{12,8},{14,10},{1,5},{3,7},... | collective-permute-start | bytes 393224 | tf_op jit(solution)/shard_map/ppermute | solution.py:27
  43.4 1.6 %collective-permute-start.20 = (f32[512,128]{1,0:T(8,128)S(1)}, f32[512,128]{1,0:T(8,128)S(1)}, u32[]{:S(2)}, u32[]{:S(2)}) collective-permute-start(f32[512,128]{1,0:T(8,128)S(1)} %fusion.2.mine_ref), channel_id=1, source_target_pairs={{0,1},{1,0},{2,3},{3,2},{4,5},{5,4},{6,7},{7,6},{8,9},{9,8},{10,11... | collective-permute-start | bytes 786440 | tf_op jit(solution)/shard_map/ppermute | solution.py:27
  45.5 5.1 %collective-permute-start.21 = (f32[72,128]{1,0:T(8,128)S(1)}, f32[72,128]{1,0:T(8,128)S(1)}, u32[]{:S(2)}, u32[]{:S(2)}) collective-permute-start(f32[72,128]{1,0:T(8,128)S(1)} %make_gram.1), channel_id=1, source_target_pairs={{1,5},{3,7},{5,1},{7,3},{9,13},{11,15},{13,9},{15,11},{17,21},{19,... | collective-permute-start | bytes 110600 | tf_op jit(solution)/shard_map/ppermute | solution.py:45
  46.2 4.5 %collective-permute-start.22 = (f32[72,128]{1,0:T(8,128)S(1)}, f32[72,128]{1,0:T(8,128)S(1)}, u32[]{:S(2)}, u32[]{:S(2)}) collective-permute-start(f32[72,128]{1,0:T(8,128)S(1)} %make_gram.1), channel_id=1, source_target_pairs={{0,2},{1,7},{2,0},{3,5},{4,6},{5,3},{6,4},{7,1},{8,10},{9,15},{10,... | collective-permute-start | bytes 110600 | tf_op jit(solution)/shard_map/ppermute | solution.py:45
  47.0 4.9 %collective-permute-start.23 = (f32[72,128]{1,0:T(8,128)S(1)}, f32[72,128]{1,0:T(8,128)S(1)}, u32[]{:S(2)}, u32[]{:S(2)}) collective-permute-start(f32[72,128]{1,0:T(8,128)S(1)} %make_gram.1), channel_id=1, source_target_pairs={{0,8},{1,13},{2,10},{3,15},{4,12},{5,9},{6,14},{7,11},{8,0},{9,5},... | collective-permute-start | bytes 110600 | tf_op jit(solution)/shard_map/ppermute | solution.py:45
  49.3 6.7 %collective-permute-start.24 = (f32[72,128]{1,0:T(8,128)S(1)}, f32[72,128]{1,0:T(8,128)S(1)}, u32[]{:S(2)}, u32[]{:S(2)}) collective-permute-start(f32[72,128]{1,0:T(8,128)S(1)} %make_gram.1), channel_id=1, source_target_pairs={{0,10},{1,15},{2,8},{3,13},{4,14},{5,11},{6,12},{7,9},{8,2},{9,7},... | collective-permute-start | bytes 110600 | tf_op jit(solution)/shard_map/ppermute | solution.py:45
  56.0 2.2 %collective-permute-start.25 = (f32[72,128]{1,0:T(8,128)S(1)}, f32[72,128]{1,0:T(8,128)S(1)}, u32[]{:S(2)}, u32[]{:S(2)}) collective-permute-start(f32[72,128]{1,0:T(8,128)S(1)} %add_add_fusion), channel_id=1, source_target_pairs={{0,1},{1,0},{2,3},{3,2},{4,5},{5,4},{6,7},{7,6},{8,9},{9,8},{10,11... | collective-permute-start | bytes 110600 | tf_op jit(solution)/shard_map/ppermute | solution.py:27
  63.1 1.0 %copy-start.2 = (f32[2,2,1,16,4096]{4,3,2,1,0:T(8,128)}, f32[2,2,1,16,4096]{4,3,2,1,0:T(8,128)S(1)}, u32[]{:S(2)}) copy-start(f32[2,2,1,16,4096]{4,3,2,1,0:T(8,128)S(1)} %get-tuple-element.17) | copy-start | bytes 3145732
  65.2 9.5 %collective-permute-start.26 = (bf16[2,2,16,4096]{3,2,0,1:T(8,128)(2,1)}, bf16[2,2,16,4096]{3,2,0,1:T(8,128)(2,1)}, u32[]{:S(2)}, u32[]{:S(2)}) collective-permute-start(bf16[2,2,16,4096]{3,2,0,1:T(8,128)(2,1)} %select_convert_fusion), channel_id=1, source_target_pairs={{0,2},{1,5},{2,0},{3,7},{4,6},{5,1},{6,4},{7,3},{8,10},{9,13},{10,... | collective-permute-start | bytes 1572872 | tf_op jit(solution)/shard_map/ppermute | solution.py:65
  76.3 1.0 %copy-start.3 = (f32[2,2,16,4096]{3,2,0,1:T(8,128)}, f32[2,2,16,4096]{3,2,0,1:T(8,128)S(1)}, u32[]{:S(2)}) copy-start(f32[2,2,16,4096]{3,2,0,1:T(8,128)S(1)} %convert_add_fusion) | copy-start | bytes 3145732
  77.4 6.4 %collective-permute-start.27 = (bf16[2,16,4096]{2,1,0:T(8,128)(2,1)S(1)}, bf16[2,16,4096]{2,1,0:T(8,128)(2,1)S(1)}, u32[]{:S(2)}, u32[]{:S(2)}) collective-permute-start(bf16[2,16,4096]{2,1,0:T(8,128)(2,1)S(1)} %fusion.13), channel_id=1, source_target_pairs={{0,4},{1,3},{2,6},{3,1},{4,0},{5,7},{6,2},{7,5},{8,12},{9,11},{10,... | collective-permute-start | bytes 786440 | tf_op jit(solution)/shard_map/ppermute | solution.py:65
  85.1 7.2 %collective-permute-start.28 = (bf16[1,16,4096]{2,1,0:T(8,128)(2,1)S(1)}, bf16[1,16,4096]{2,1,0:T(8,128)(2,1)S(1)}, u32[]{:S(2)}, u32[]{:S(2)}) collective-permute-start(bf16[1,16,4096]{2,1,0:T(8,128)(2,1)S(1)} %fusion.28), channel_id=1, source_target_pairs={{0,8},{1,9},{2,10},{3,11},{4,12},{5,13},{6,14},{7,15},{8,0},{9,1},... | collective-permute-start | bytes 393224 | tf_op jit(solution)/shard_map/ppermute | solution.py:65

commit v15 on v13

--- a/solution.py
+++ b/solution.py
@@ -8,18 +8,9 @@
 from jax.experimental.pallas import tpu as pltpu
 from jax.sharding import PartitionSpec as P
 
-SKETCH_CHUNKS = 4
+CHUNKS = 4
 TILE = 512
 KERNEL_VMEM = 50 * 2**20
-
-
-def levels_of(size):
-    levels, stride = [], 1
-    while stride < size:
-        radix = 2 if stride == 1 else min(4, size // stride)
-        levels.append((stride, radix))
-        stride *= radix
-    return levels
 
 
 def swap(value, axis, distance):
@@ -51,26 +42,20 @@
     return value
 
 
-def digit_of(axis, stride, radix):
-    return lax.rem(lax.div(lax.axis_index(axis), stride), radix)
-
-
-def scatter_sum(value, axis, reverse):
-    levels = levels_of(lax.axis_size(axis))
-    rows = value.shape[0] // lax.axis_size(axis)
-    total = value.reshape([radix for _, radix in reversed(levels)] + [rows, value.shape[1]])
-    order = range(len(levels))
-    for level in reversed(order) if reverse else order:
-        stride, radix = levels[level]
-        dim = len(levels) - 1 - level
-        digit = digit_of(axis, stride, radix)
-        parts = total
-        total = lax.dynamic_slice_in_dim(parts, digit, 1, dim)
-        for t in range(1, radix):
-            part = lax.dynamic_slice_in_dim(parts, jnp.bitwise_xor(digit, t), 1, dim)
-            landed = swap(part.astype(jnp.bfloat16), axis, t * stride)
-            total = total + landed.astype(jnp.float32)
-    return total.reshape(rows, value.shape[1])
+def scatter_sum(value, axis, order):
+    rows, cols = value.shape[0] >> len(order), value.shape[1]
+    total = value.reshape([2] * len(order) + [rows, cols])
+    left = sorted(order, reverse=True)
+    for bit in order:
+        dim = left.index(bit)
+        left.remove(bit)
+        low = lax.index_in_dim(total, 0, dim, keepdims=False)
+        high = lax.index_in_dim(total, 1, dim, keepdims=False)
+        upper = bit_of(axis, bit) == 1
+        send = jnp.where(upper, low, high).astype(jnp.bfloat16)
+        landed = swap(send, axis, 1 << bit)
+        total = jnp.where(upper, high, low) + landed.astype(jnp.float32)
+    return total
 
 
 def bit_of(axis, bit):
@@ -219,8 +204,9 @@
 
 def basis_kernel(
     total_cols, root_rows, gram_ref, mine_ref, other_ref, slab_ref,
-    basis_ref, product_ref, work_ref, inverse_ref, buffer, arrived,
+    basis_ref, *refs,
 ):
+    products, (work_ref, inverse_ref, buffer, arrived) = refs[:-4], refs[-4:]
     fetch = pltpu.make_async_copy(slab_ref, buffer, arrived)
     fetch.start()
     width = gram_ref.shape[1]
@@ -282,20 +268,20 @@
             (((1,), (0,)), ((), ())),
             preferred_element_type=jnp.float32,
         )
-        product_ref[:, start : start + TILE] = both[:width] + both[width:]
-
-
-def make_basis(gram, mine, other, slab, total_cols, root_rows):
+        out, inner = divmod(start, products[0].shape[1])
+        products[out][:, inner : inner + TILE] = both[:width] + both[width:]
+
+
+def make_basis(gram, mine, other, slab, total_cols, root_rows, chunks):
     rows, width = mine.shape
+    cols = slab.shape[1]
     return pl.pallas_call(
         functools.partial(basis_kernel, total_cols, root_rows),
-        out_shape=(
-            jax.ShapeDtypeStruct((rows, width), jnp.float32),
-            jax.ShapeDtypeStruct((width, slab.shape[1]), jnp.float32),
-        ),
+        out_shape=[jax.ShapeDtypeStruct((rows, width), jnp.float32)]
+        + [jax.ShapeDtypeStruct((width, cols // chunks), jnp.float32)] * chunks,
         in_specs=[pl.BlockSpec(memory_space=pltpu.VMEM)] * 3
         + [pl.BlockSpec(memory_space=pl.ANY)],
-        out_specs=[pl.BlockSpec(memory_space=pltpu.VMEM)] * 2,
+        out_specs=[pl.BlockSpec(memory_space=pltpu.VMEM)] * (1 + chunks),
         scratch_shapes=[
             pltpu.VMEM((width, width), jnp.float32),
             pltpu.VMEM((width, width), jnp.float32),
@@ -315,11 +301,11 @@
     total_cols = cols_here * lax.axis_size("col")
     root_rows = math.sqrt(total_rows)
 
-    local_cols = first_product(start_sketch, activations, SKETCH_CHUNKS)
+    local_cols = first_product(start_sketch, activations, CHUNKS)
     partial_sketch = 0.0
     orders = orders_of("row")
-    step = cols_here // SKETCH_CHUNKS
-    for c in range(SKETCH_CHUNKS):
+    step = cols_here // CHUNKS
+    for c in range(CHUNKS):
         span = slice(c * step, (c + 1) * step)
         shared = sum_and_share(local_cols[c], "row", orders[c % 2], 1.0 / root_rows)
         partial_sketch = partial_sketch + lax.dot_general(
@@ -330,14 +316,13 @@
         )
     other_sketch = swap(partial_sketch, "col", 1)
     gram = row_sum(make_gram(partial_sketch, other_sketch, total_cols))
-    basis, local_proj = make_basis(
-        gram, partial_sketch, other_sketch, activations, total_cols, root_rows
+    basis, *products = make_basis(
+        gram, partial_sketch, other_sketch, activations, total_cols, root_rows, CHUNKS
     )
 
-    cut = cols_here * 5 // 8
     pieces = [
-        scatter_sum(local_proj[:, :cut], "row", False) / total_rows,
-        scatter_sum(local_proj[:, cut:], "row", True) / total_rows,
+        scatter_sum(product, "row", orders[c % 2]) / total_rows
+        for c, product in enumerate(products)
     ]
     return (basis, jnp.concatenate(pieces, axis=1))
 

time: 84.6 us -> 82.8 us (0.979)
  waiting for transfers between devices: 27.4 us -> 19.5 us
  starting transfers between devices: 43.3 us -> 49 us
    ppermute x30 -> x34, waiting for transfers between devices: 23.9 us -> 17 us  [swap(): return lax.ppermute(value, axis, [(i, i ^ distance) for i in range(size)])]
    ppermute x30 -> x34, starting transfers between devices: 38.2 us -> 43.9 us  [swap(): return lax.ppermute(value, axis, [(i, i ^ distance) for i in range(size)])]
    ppermute x4, waiting for transfers between devices: 3.45 us -> 2.47 us  [row_sum(): terms.append(lax.ppermute(value, ('row', 'col'), pairs))]
  transfers between devices with their start and end apart: 34 -> 38, of which waited for: 19 -> 18; matrix products, arithmetic and copies ran while one was open for 3% -> 3% of each run, Pallas kernels for 0% -> 0%
where the time goes in v15:
time: 82.8 us; the launch traced here: 82.6 us
  starting transfers between devices  49 us (59%)
  waiting for transfers between devices  19.5 us (24%)
  Pallas kernels  8.11 us (10%)
  other arithmetic  2.14 us (3%)
  matrix products  1.74 us (2%)
  between operations  1.1 us (1%)
  local copies, waits for them, and re-layouts  1.05 us (1%)
    ppermute x34, starting transfers between devices, swap(): return lax.ppermute(value, axis, [(i, i ^ distance) for i in range(size)])  43.9 us
    ppermute x34, waiting for transfers between devices, swap(): return lax.ppermute(value, axis, [(i, i ^ distance) for i in range(size)])  17 us
    ppermute x4, starting transfers between devices, row_sum(): terms.append(lax.ppermute(value, ('row', 'col'), pairs))  5.1 us
    pallas_call x1, Pallas kernels, make_basis(): pl.pallas_call(functools.partial(basis_kernel, total_cols, root_rows), ou...  4.63 us
    pallas_call x1, Pallas kernels, first_product(): pl.pallas_call(sketch_kernel, out_shape=[jax.ShapeDtypeStruct((width, col...  2.99 us
    ppermute x4, waiting for transfers between devices, row_sum(): terms.append(lax.ppermute(value, ('row', 'col'), pairs))  2.47 us
    dot_general x4, matrix products, per_device(): lax.dot_general(activations[:, span], shared, (((1,), (1,)), ((), ())), p...  1.74 us
  transfers between devices with their start and end apart: 38, of which 18 were waited for; matrix products, arithmetic and copies ran while one was open for 3% of the time, Pallas kernels for 0%

profile of v15, /device:TPU:0, one launch (start us, length us, event | category | flops | bytes accessed | tf_op | source)
XLA Modules:
  0.0 82.6 jit_solution(3340766594086282429)
XLA Ops:
  0.7 0.9 %copy-done = bf16[512,128]{1,0:T(8,128)(2,1)S(1)} copy-done((bf16[512,128]{1,0:T(8,128)(2,1)S(1)}, bf16[512,128]{1,0:T(8,128)(2,1)}, u32[]{:S(2)}) %copy-start) | copy-done | bytes 131096
  1.6 3.0 %first_product.1 = (f32[128,1024]{1,0:T(8,128)S(1)}, f32[128,1024]{1,0:T(8,128)S(1)}, f32[128,1024]{1,0:T(8,128)S(1)}, f32[128,1024]{1,0:T(8,128)S(1)}) custom-call(bf16[512,128]{1,0:T(8,128)(2,1)S(1)} %copy-done, bf16[512,4096]{1,0:T(8,128)(2,1)} %slab_ref.3), custom_call_target="tpu_custom_call" | custom-call | flops 536870912 | bytes 4194304 | tf_op jit(solution)/shard_map/first_product/pallas_call | solution.py:118
  4.6 3.1 %collective-permute-start.15 = (bf16[128,512]{1,0:T(8,128)(2,1)S(1)}, bf16[128,512]{1,0:T(8,128)(2,1)S(1)}, u32[]{:S(2)}, u32[]{:S(2)}) collective-permute-start(bf16[128,512]{1,0:T(8,128)(2,1)S(1)} %select_convert_fusion.4), channel_id=1, source_target_pairs={{0,4},{2,6},{4,0},{6,2},{8,12},{10,14},{12,8},{14,10},{1,5},{3,7},... | collective-permute-start | bytes 393224 | tf_op jit(solution)/shard_map/ppermute | solution.py:18
  7.7 1.6 %collective-permute-start.10 = (bf16[128,512]{1,0:T(8,128)(2,1)S(1)}, bf16[128,512]{1,0:T(8,128)(2,1)S(1)}, u32[]{:S(2)}, u32[]{:S(2)}) collective-permute-start(bf16[128,512]{1,0:T(8,128)(2,1)S(1)} %select_convert_fusion.5), channel_id=1, source_target_pairs={{0,2},{2,0},{4,6},{6,4},{8,10},{10,8},{12,14},{14,12},{1,3},{3,1},... | collective-permute-start | bytes 393224 | tf_op jit(solution)/shard_map/ppermute | solution.py:18
  10.0 1.6 %collective-permute-done.15 = bf16[128,512]{1,0:T(8,128)(2,1)S(1)} collective-permute-done((bf16[128,512]{1,0:T(8,128)(2,1)S(1)}, bf16[128,512]{1,0:T(8,128)(2,1)S(1)}, u32[]{:S(2)}, u32[]{:S(2)}) %collective-permute-start.15) | collective-permute-done | bytes 131104 | tf_op jit(solution)/shard_map/ppermute | solution.py:18
  11.7 2.4 %collective-permute-start.16 = (bf16[128,256]{1,0:T(8,128)(2,1)S(1)}, bf16[128,256]{1,0:T(8,128)(2,1)S(1)}, u32[]{:S(2)}, u32[]{:S(2)}) collective-permute-start(bf16[128,256]{1,0:T(8,128)(2,1)S(1)} %select_convert_fusion.12), channel_id=1, source_target_pairs={{0,2},{2,0},{4,6},{6,4},{8,10},{10,8},{12,14},{14,12},{1,3},{3,1},... | collective-permute-start | bytes 196616 | tf_op jit(solution)/shard_map/ppermute | solution.py:18
  14.1 1.7 %collective-permute-start.11 = (bf16[128,256]{1,0:T(8,128)(2,1)S(1)}, bf16[128,256]{1,0:T(8,128)(2,1)S(1)}, u32[]{:S(2)}, u32[]{:S(2)}) collective-permute-start(bf16[128,256]{1,0:T(8,128)(2,1)S(1)} %select_convert_fusion.13), channel_id=1, source_target_pairs={{0,4},{2,6},{4,0},{6,2},{8,12},{10,14},{12,8},{14,10},{1,5},{3,7},... | collective-permute-start | bytes 196616 | tf_op jit(solution)/shard_map/ppermute | solution.py:18
  16.7 1.5 %collective-permute-start.1 = (bf16[128,256]{1,0:T(8,128)(2,1)S(1)}, bf16[128,256]{1,0:T(8,128)(2,1)S(1)}, u32[]{:S(2)}, u32[]{:S(2)}) collective-permute-start(bf16[128,256]{1,0:T(8,128)(2,1)S(1)} %select_convert_fusion.15), channel_id=1, source_target_pairs={{0,4},{2,6},{4,0},{6,2},{8,12},{10,14},{12,8},{14,10},{1,5},{3,7},... | collective-permute-start | bytes 196616 | tf_op jit(solution)/shard_map/ppermute | solution.py:18
  18.2 2.7 %collective-permute-start.17 = (bf16[128,256]{1,0:T(8,128)(2,1)S(1)}, bf16[128,256]{1,0:T(8,128)(2,1)S(1)}, u32[]{:S(2)}, u32[]{:S(2)}) collective-permute-start(bf16[128,256]{1,0:T(8,128)(2,1)S(1)} %fusion.41), channel_id=1, source_target_pairs={{0,8},{2,10},{4,12},{6,14},{8,0},{10,2},{12,4},{14,6},{1,9},{3,11}... | collective-permute-start | bytes 196616 | tf_op jit(solution)/shard_map/ppermute | solution.py:18
  20.9 0.9 %collective-permute-start.12 = (bf16[128,256]{1,0:T(8,128)(2,1)S(1)}, bf16[128,256]{1,0:T(8,128)(2,1)S(1)}, u32[]{:S(2)}, u32[]{:S(2)}) collective-permute-start(bf16[128,256]{1,0:T(8,128)(2,1)S(1)} %fusion.40), channel_id=1, source_target_pairs={{0,8},{2,10},{4,12},{6,14},{8,0},{10,2},{12,4},{14,6},{1,9},{3,11}... | collective-permute-start | bytes 196616 | tf_op jit(solution)/shard_map/ppermute | solution.py:18
  21.8 2.2 %collective-permute-start.7 = (bf16[128,256]{1,0:T(8,128)(2,1)S(1)}, bf16[128,256]{1,0:T(8,128)(2,1)S(1)}, u32[]{:S(2)}, u32[]{:S(2)}) collective-permute-start(bf16[128,256]{1,0:T(8,128)(2,1)S(1)} %fusion.39), channel_id=1, source_target_pairs={{0,8},{2,10},{4,12},{6,14},{8,0},{10,2},{12,4},{14,6},{1,9},{3,11}... | collective-permute-start | bytes 196616 | tf_op jit(solution)/shard_map/ppermute | solution.py:18
  24.0 0.9 %collective-permute-start.2 = (bf16[128,256]{1,0:T(8,128)(2,1)S(1)}, bf16[128,256]{1,0:T(8,128)(2,1)S(1)}, u32[]{:S(2)}, u32[]{:S(2)}) collective-permute-start(bf16[128,256]{1,0:T(8,128)(2,1)S(1)} %fusion.38), channel_id=1, source_target_pairs={{0,8},{2,10},{4,12},{6,14},{8,0},{10,2},{12,4},{14,6},{1,9},{3,11}... | collective-permute-start | bytes 196616 | tf_op jit(solution)/shard_map/ppermute | solution.py:18
  24.9 2.2 %collective-permute-done.17 = bf16[128,256]{1,0:T(8,128)(2,1)S(1)} collective-permute-done((bf16[128,256]{1,0:T(8,128)(2,1)S(1)}, bf16[128,256]{1,0:T(8,128)(2,1)S(1)}, u32[]{:S(2)}, u32[]{:S(2)}) %collective-permute-start.17) | collective-permute-done | bytes 65568 | tf_op jit(solution)/shard_map/ppermute | solution.py:18
  27.1 1.8 %collective-permute-start.18 = (bf16[128,256]{1,0:T(8,128)(2,1)S(1)}, bf16[128,256]{1,0:T(8,128)(2,1)S(1)}, u32[]{:S(2)}, u32[]{:S(2)}) collective-permute-start(bf16[128,256]{1,0:T(8,128)(2,1)S(1)} %multiply_convert_fusion), channel_id=1, source_target_pairs={{0,2},{2,0},{4,6},{6,4},{8,10},{10,8},{12,14},{14,12},{1,3},{3,1},... | collective-permute-start | bytes 196616 | tf_op jit(solution)/shard_map/ppermute | solution.py:18
  28.9 1.1 %collective-permute-done.12 = bf16[128,256]{1,0:T(8,128)(2,1)S(1)} collective-permute-done((bf16[128,256]{1,0:T(8,128)(2,1)S(1)}, bf16[128,256]{1,0:T(8,128)(2,1)S(1)}, u32[]{:S(2)}, u32[]{:S(2)}) %collective-permute-start.12) | collective-permute-done | bytes 65568 | tf_op jit(solution)/shard_map/ppermute | solution.py:18
  30.1 1.0 %collective-permute-done.7 = bf16[128,256]{1,0:T(8,128)(2,1)S(1)} collective-permute-done((bf16[128,256]{1,0:T(8,128)(2,1)S(1)}, bf16[128,256]{1,0:T(8,128)(2,1)S(1)}, u32[]{:S(2)}, u32[]{:S(2)}) %collective-permute-start.7) | collective-permute-done | bytes 65568 | tf_op jit(solution)/shard_map/ppermute | solution.py:18
  31.1 1.2 %collective-permute-start.8 = (bf16[128,256]{1,0:T(8,128)(2,1)S(1)}, bf16[128,256]{1,0:T(8,128)(2,1)S(1)}, u32[]{:S(2)}, u32[]{:S(2)}) collective-permute-start(bf16[128,256]{1,0:T(8,128)(2,1)S(1)} %multiply_convert_fusion.2), channel_id=1, source_target_pairs={{0,2},{2,0},{4,6},{6,4},{8,10},{10,8},{12,14},{14,12},{1,3},{3,1},... | collective-permute-start | bytes 196616 | tf_op jit(solution)/shard_map/ppermute | solution.py:18
  32.3 1.1 %collective-permute-start.3 = (bf16[128,256]{1,0:T(8,128)(2,1)S(1)}, bf16[128,256]{1,0:T(8,128)(2,1)S(1)}, u32[]{:S(2)}, u32[]{:S(2)}) collective-permute-start(bf16[128,256]{1,0:T(8,128)(2,1)S(1)} %multiply_convert_fusion.3), channel_id=1, source_target_pairs={{0,4},{2,6},{4,0},{6,2},{8,12},{10,14},{12,8},{14,10},{1,5},{3,7},... | collective-permute-start | bytes 196616 | tf_op jit(solution)/shard_map/ppermute | solution.py:18
  33.5 1.0 %collective-permute-start.19 = (bf16[128,512]{1,0:T(8,128)(2,1)S(1)}, bf16[128,512]{1,0:T(8,128)(2,1)S(1)}, u32[]{:S(2)}, u32[]{:S(2)}) collective-permute-start(bf16[128,512]{1,0:T(8,128)(2,1)S(1)} %pad_maximum_fusion.4), channel_id=1, source_target_pairs={{0,4},{2,6},{4,0},{6,2},{8,12},{10,14},{12,8},{14,10},{1,5},{3,7},... | collective-permute-start | bytes 393224 | tf_op jit(solution)/shard_map/ppermute | solution.py:18
  35.0 1.2 %collective-permute-start.14 = (bf16[128,512]{1,0:T(8,128)(2,1)S(1)}, bf16[128,512]{1,0:T(8,128)(2,1)S(1)}, u32[]{:S(2)}, u32[]{:S(2)}) collective-permute-start(bf16[128,512]{1,0:T(8,128)(2,1)S(1)} %pad_maximum_fusion.3), channel_id=1, source_target_pairs={{0,2},{2,0},{4,6},{6,4},{8,10},{10,8},{12,14},{14,12},{1,3},{3,1},... | collective-permute-start | bytes 393224 | tf_op jit(solution)/shard_map/ppermute | solution.py:18
  36.3 0.9 %collective-permute-start.9 = (bf16[128,512]{1,0:T(8,128)(2,1)S(1)}, bf16[128,512]{1,0:T(8,128)(2,1)S(1)}, u32[]{:S(2)}, u32[]{:S(2)}) collective-permute-start(bf16[128,512]{1,0:T(8,128)(2,1)S(1)} %pad_maximum_fusion.2), channel_id=1, source_target_pairs={{0,4},{2,6},{4,0},{6,2},{8,12},{10,14},{12,8},{14,10},{1,5},{3,7},... | collective-permute-start | bytes 393224 | tf_op jit(solution)/shard_map/ppermute | solution.py:18
  37.5 1.1 %collective-permute-start.4 = (bf16[128,512]{1,0:T(8,128)(2,1)S(1)}, bf16[128,512]{1,0:T(8,128)(2,1)S(1)}, u32[]{:S(2)}, u32[]{:S(2)}) collective-permute-start(bf16[128,512]{1,0:T(8,128)(2,1)S(1)} %pad_maximum_fusion.1), channel_id=1, source_target_pairs={{0,2},{2,0},{4,6},{6,4},{8,10},{10,8},{12,14},{14,12},{1,3},{3,1},... | collective-permute-start | bytes 393224 | tf_op jit(solution)/shard_map/ppermute | solution.py:18
  38.5 1.4 %collective-permute-done.19 = bf16[128,512]{1,0:T(8,128)(2,1)S(1)} collective-permute-done((bf16[128,512]{1,0:T(8,128)(2,1)S(1)}, bf16[128,512]{1,0:T(8,128)(2,1)S(1)}, u32[]{:S(2)}, u32[]{:S(2)}) %collective-permute-start.19) | collective-permute-done | bytes 131104 | tf_op jit(solution)/shard_map/ppermute | solution.py:18
  43.1 1.5 %collective-permute-done.20.other_ref = f32[512,128]{1,0:T(8,128)S(1)} collective-permute-done((f32[512,128]{1,0:T(8,128)S(1)}, f32[512,128]{1,0:T(8,128)S(1)}, u32[]{:S(2)}, u32[]{:S(2)}) %collective-permute-start.20) | collective-permute-done | bytes 262176 | tf_op jit(solution)/shard_map/ppermute | solution.py:18
  45.1 2.0 %collective-permute-start.24 = (f32[72,128]{1,0:T(8,128)S(1)}, f32[72,128]{1,0:T(8,128)S(1)}, u32[]{:S(2)}, u32[]{:S(2)}) collective-permute-start(f32[72,128]{1,0:T(8,128)S(1)} %make_gram.1), channel_id=1, source_target_pairs={{0,10},{1,15},{2,8},{3,13},{4,14},{5,11},{6,12},{7,9},{8,2},{9,7},... | collective-permute-start | bytes 110600 | tf_op jit(solution)/shard_map/ppermute | solution.py:36
  47.1 1.4 %collective-permute-start.23 = (f32[72,128]{1,0:T(8,128)S(1)}, f32[72,128]{1,0:T(8,128)S(1)}, u32[]{:S(2)}, u32[]{:S(2)}) collective-permute-start(f32[72,128]{1,0:T(8,128)S(1)} %make_gram.1), channel_id=1, source_target_pairs={{0,8},{1,13},{2,10},{3,15},{4,12},{5,9},{6,14},{7,11},{8,0},{9,5},... | collective-permute-start | bytes 110600 | tf_op jit(solution)/shard_map/ppermute | solution.py:36
  48.5 1.0 %collective-permute-start.22 = (f32[72,128]{1,0:T(8,128)S(1)}, f32[72,128]{1,0:T(8,128)S(1)}, u32[]{:S(2)}, u32[]{:S(2)}) collective-permute-start(f32[72,128]{1,0:T(8,128)S(1)} %make_gram.1), channel_id=1, source_target_pairs={{0,2},{1,7},{2,0},{3,5},{4,6},{5,3},{6,4},{7,1},{8,10},{9,15},{10,... | collective-permute-start | bytes 110600 | tf_op jit(solution)/shard_map/ppermute | solution.py:36
  49.5 0.7 collective-permute-start.21
  50.2 1.7 %collective-permute-done.24 = f32[72,128]{1,0:T(8,128)S(1)} collective-permute-done((f32[72,128]{1,0:T(8,128)S(1)}, f32[72,128]{1,0:T(8,128)S(1)}, u32[]{:S(2)}, u32[]{:S(2)}) %collective-permute-start.24) | collective-permute-done | bytes 36896 | tf_op jit(solution)/shard_map/ppermute | solution.py:36
  51.9 0.8 collective-permute-done.23
  52.7 1.5 %collective-permute-start.25 = (f32[72,128]{1,0:T(8,128)S(1)}, f32[72,128]{1,0:T(8,128)S(1)}, u32[]{:S(2)}, u32[]{:S(2)}) collective-permute-start(f32[72,128]{1,0:T(8,128)S(1)} %add_add_fusion), channel_id=1, source_target_pairs={{0,1},{1,0},{2,3},{3,2},{4,5},{5,4},{6,7},{7,6},{8,9},{9,8},{10,11... | collective-permute-start | bytes 110600 | tf_op jit(solution)/shard_map/ppermute | solution.py:18
  54.2 0.9 %collective-permute-done.25 = f32[72,128]{1,0:T(8,128)S(1)} collective-permute-done((f32[72,128]{1,0:T(8,128)S(1)}, f32[72,128]{1,0:T(8,128)S(1)}, u32[]{:S(2)}, u32[]{:S(2)}) %collective-permute-start.25) | collective-permute-done | bytes 36896 | tf_op jit(solution)/shard_map/ppermute | solution.py:18
  55.1 4.6 %make_basis.1 = (f32[512,128]{1,0:T(8,128)}, f32[128,1024]{1,0:T(8,128)S(1)}, f32[128,1024]{1,0:T(8,128)S(1)}, f32[128,1024]{1,0:T(8,128)S(1)}, f32[128,1024]{1,0:T(8,128)S(1)}) custom-call(f32[72,128]{1,0:T(8,128)S(1)} %add.116.gram_ref, f32[512,128]{1,0:T(8,128)S(1)} %fusion.2.mine_ref, f32[512,128]{1,0:T(8,128)S(1)} %collective-permute-done.20.other_ref, ...), custom_call_target="tpu_custom_call" | custom-call | tf_op jit(solution)/shard_map/make_basis/pallas_call | solution.py:278
  59.8 1.1 %collective-permute-start.26 = (bf16[2,2,16,1024]{3,2,0,1:T(8,128)(2,1)S(1)}, bf16[2,2,16,1024]{3,2,0,1:T(8,128)(2,1)S(1)}, u32[]{:S(2)}, u32[]{:S(2)}) collective-permute-start(bf16[2,2,16,1024]{3,2,0,1:T(8,128)(2,1)S(1)} %fusion.22), channel_id=1, source_target_pairs={{0,2},{2,0},{4,6},{6,4},{8,10},{10,8},{12,14},{14,12},{1,3},{3,1},... | collective-permute-start | bytes 393224 | tf_op jit(solution)/shard_map/ppermute | solution.py:18
  61.0 1.8 %collective-permute-start.29 = (bf16[2,2,16,1024]{3,2,0,1:T(8,128)(2,1)S(1)}, bf16[2,2,16,1024]{3,2,0,1:T(8,128)(2,1)S(1)}, u32[]{:S(2)}, u32[]{:S(2)}) collective-permute-start(bf16[2,2,16,1024]{3,2,0,1:T(8,128)(2,1)S(1)} %fusion.23), channel_id=1, source_target_pairs={{0,4},{2,6},{4,0},{6,2},{8,12},{10,14},{12,8},{14,10},{1,5},{3,7},... | collective-permute-start | bytes 393224 | tf_op jit(solution)/shard_map/ppermute | solution.py:18
  62.8 1.1 %collective-permute-start.32 = (bf16[2,2,16,1024]{3,2,0,1:T(8,128)(2,1)S(1)}, bf16[2,2,16,1024]{3,2,0,1:T(8,128)(2,1)S(1)}, u32[]{:S(2)}, u32[]{:S(2)}) collective-permute-start(bf16[2,2,16,1024]{3,2,0,1:T(8,128)(2,1)S(1)} %fusion.24), channel_id=1, source_target_pairs={{0,2},{2,0},{4,6},{6,4},{8,10},{10,8},{12,14},{14,12},{1,3},{3,1},... | collective-permute-start | bytes 393224 | tf_op jit(solution)/shard_map/ppermute | solution.py:18
  64.4 1.6 %collective-permute-done.26 = bf16[2,2,16,1024]{3,2,0,1:T(8,128)(2,1)S(1)} collective-permute-done((bf16[2,2,16,1024]{3,2,0,1:T(8,128)(2,1)S(1)}, bf16[2,2,16,1024]{3,2,0,1:T(8,128)(2,1)S(1)}, u32[]{:S(2)}, u32[]{:S(2)}) %collective-permute-start.26) | collective-permute-done | bytes 131104 | tf_op jit(solution)/shard_map/ppermute | solution.py:18
  66.0 2.1 %collective-permute-start.27 = (bf16[2,16,1024]{2,1,0:T(8,128)(2,1)S(1)}, bf16[2,16,1024]{2,1,0:T(8,128)(2,1)S(1)}, u32[]{:S(2)}, u32[]{:S(2)}) collective-permute-start(bf16[2,16,1024]{2,1,0:T(8,128)(2,1)S(1)} %fusion.26), channel_id=1, source_target_pairs={{0,4},{2,6},{4,0},{6,2},{8,12},{10,14},{12,8},{14,10},{1,5},{3,7},... | collective-permute-start | bytes 196616 | tf_op jit(solution)/shard_map/ppermute | solution.py:18
  68.2 1.1 %collective-permute-start.30 = (bf16[2,16,1024]{2,1,0:T(8,128)(2,1)S(1)}, bf16[2,16,1024]{2,1,0:T(8,128)(2,1)S(1)}, u32[]{:S(2)}, u32[]{:S(2)}) collective-permute-start(bf16[2,16,1024]{2,1,0:T(8,128)(2,1)S(1)} %fusion.27), channel_id=1, source_target_pairs={{0,2},{2,0},{4,6},{6,4},{8,10},{10,8},{12,14},{14,12},{1,3},{3,1},... | collective-permute-start | bytes 196616 | tf_op jit(solution)/shard_map/ppermute | solution.py:18
  69.3 1.1 %collective-permute-start.33 = (bf16[2,16,1024]{2,1,0:T(8,128)(2,1)S(1)}, bf16[2,16,1024]{2,1,0:T(8,128)(2,1)S(1)}, u32[]{:S(2)}, u32[]{:S(2)}) collective-permute-start(bf16[2,16,1024]{2,1,0:T(8,128)(2,1)S(1)} %fusion.28), channel_id=1, source_target_pairs={{0,4},{2,6},{4,0},{6,2},{8,12},{10,14},{12,8},{14,10},{1,5},{3,7},... | collective-permute-start | bytes 196616 | tf_op jit(solution)/shard_map/ppermute | solution.py:18
  70.5 1.1 %collective-permute-start.36 = (bf16[2,16,1024]{2,1,0:T(8,128)(2,1)S(1)}, bf16[2,16,1024]{2,1,0:T(8,128)(2,1)S(1)}, u32[]{:S(2)}, u32[]{:S(2)}) collective-permute-start(bf16[2,16,1024]{2,1,0:T(8,128)(2,1)S(1)} %fusion.29), channel_id=1, source_target_pairs={{0,2},{2,0},{4,6},{6,4},{8,10},{10,8},{12,14},{14,12},{1,3},{3,1},... | collective-permute-start | bytes 196616 | tf_op jit(solution)/shard_map/ppermute | solution.py:18
  71.6 1.9 %collective-permute-start.28 = (bf16[16,1024]{1,0:T(8,128)(2,1)S(1)}, bf16[16,1024]{1,0:T(8,128)(2,1)S(1)}, u32[]{:S(2)}, u32[]{:S(2)}) collective-permute-start(bf16[16,1024]{1,0:T(8,128)(2,1)S(1)} %fusion.34), channel_id=1, source_target_pairs={{0,8},{2,10},{4,12},{6,14},{8,0},{10,2},{12,4},{14,6},{1,9},{3,11}... | collective-permute-start | bytes 98312 | tf_op jit(solution)/shard_map/ppermute | solution.py:18
  73.5 1.2 %collective-permute-start.31 = (bf16[16,1024]{1,0:T(8,128)(2,1)S(1)}, bf16[16,1024]{1,0:T(8,128)(2,1)S(1)}, u32[]{:S(2)}, u32[]{:S(2)}) collective-permute-start(bf16[16,1024]{1,0:T(8,128)(2,1)S(1)} %fusion.35), channel_id=1, source_target_pairs={{0,8},{2,10},{4,12},{6,14},{8,0},{10,2},{12,4},{14,6},{1,9},{3,11}... | collective-permute-start | bytes 98312 | tf_op jit(solution)/shard_map/ppermute | solution.py:18
  74.8 1.9 %collective-permute-start.34 = (bf16[16,1024]{1,0:T(8,128)(2,1)S(1)}, bf16[16,1024]{1,0:T(8,128)(2,1)S(1)}, u32[]{:S(2)}, u32[]{:S(2)}) collective-permute-start(bf16[16,1024]{1,0:T(8,128)(2,1)S(1)} %fusion.36), channel_id=1, source_target_pairs={{0,8},{2,10},{4,12},{6,14},{8,0},{10,2},{12,4},{14,6},{1,9},{3,11}... | collective-permute-start | bytes 98312 | tf_op jit(solution)/shard_map/ppermute | solution.py:18
  76.7 1.2 %collective-permute-start.37 = (bf16[16,1024]{1,0:T(8,128)(2,1)S(1)}, bf16[16,1024]{1,0:T(8,128)(2,1)S(1)}, u32[]{:S(2)}, u32[]{:S(2)}) collective-permute-start(bf16[16,1024]{1,0:T(8,128)(2,1)S(1)} %fusion.37), channel_id=1, source_target_pairs={{0,8},{2,10},{4,12},{6,14},{8,0},{10,2},{12,4},{14,6},{1,9},{3,11}... | collective-permute-start | bytes 98312 | tf_op jit(solution)/shard_map/ppermute | solution.py:18
  77.9 1.4 %collective-permute-done.31 = bf16[16,1024]{1,0:T(8,128)(2,1)S(1)} collective-permute-done((bf16[16,1024]{1,0:T(8,128)(2,1)S(1)}, bf16[16,1024]{1,0:T(8,128)(2,1)S(1)}, u32[]{:S(2)}, u32[]{:S(2)}) %collective-permute-start.31) | collective-permute-done | bytes 32800 | tf_op jit(solution)/shard_map/ppermute | solution.py:18
  79.7 2.2 %collective-permute-done.37 = bf16[16,1024]{1,0:T(8,128)(2,1)S(1)} collective-permute-done((bf16[16,1024]{1,0:T(8,128)(2,1)S(1)}, bf16[16,1024]{1,0:T(8,128)(2,1)S(1)}, u32[]{:S(2)}, u32[]{:S(2)}) %collective-permute-start.37) | collective-permute-done | bytes 32800 | tf_op jit(solution)/shard_map/ppermute | solution.py:18
  81.9 0.7 pad_maximum_fusion
  (102 shorter events, 7.8 us)
Async XLA Ops:
  0.6 0.9 %copy-start = (bf16[512,128]{1,0:T(8,128)(2,1)S(1)}, bf16[512,128]{1,0:T(8,128)(2,1)}, u32[]{:S(2)}) copy-start(bf16[512,128]{1,0:T(8,128)(2,1)} %start_ref.1) | copy-start | bytes 393220
  4.6 7.0 %collective-permute-start.15 = (bf16[128,512]{1,0:T(8,128)(2,1)S(1)}, bf16[128,512]{1,0:T(8,128)(2,1)S(1)}, u32[]{:S(2)}, u32[]{:S(2)}) collective-permute-start(bf16[128,512]{1,0:T(8,128)(2,1)S(1)} %select_convert_fusion.4), channel_id=1, source_target_pairs={{0,4},{2,6},{4,0},{6,2},{8,12},{10,14},{12,8},{14,10},{1,5},{3,7},... | collective-permute-start | bytes 393224 | tf_op jit(solution)/shard_map/ppermute | solution.py:18
  7.7 6.3 %collective-permute-start.10 = (bf16[128,512]{1,0:T(8,128)(2,1)S(1)}, bf16[128,512]{1,0:T(8,128)(2,1)S(1)}, u32[]{:S(2)}, u32[]{:S(2)}) collective-permute-start(bf16[128,512]{1,0:T(8,128)(2,1)S(1)} %select_convert_fusion.5), channel_id=1, source_target_pairs={{0,2},{2,0},{4,6},{6,4},{8,10},{10,8},{12,14},{14,12},{1,3},{3,1},... | collective-permute-start | bytes 393224 | tf_op jit(solution)/shard_map/ppermute | solution.py:18
  9.3 6.6 %collective-permute-start.5 = (bf16[128,512]{1,0:T(8,128)(2,1)S(1)}, bf16[128,512]{1,0:T(8,128)(2,1)S(1)}, u32[]{:S(2)}, u32[]{:S(2)}) collective-permute-start(bf16[128,512]{1,0:T(8,128)(2,1)S(1)} %select_convert_fusion.6), channel_id=1, source_target_pairs={{0,4},{2,6},{4,0},{6,2},{8,12},{10,14},{12,8},{14,10},{1,5},{3,7},... | collective-permute-start | bytes 393224 | tf_op jit(solution)/shard_map/ppermute | solution.py:18
  9.8 6.7 %collective-permute-start = (bf16[128,512]{1,0:T(8,128)(2,1)S(1)}, bf16[128,512]{1,0:T(8,128)(2,1)S(1)}, u32[]{:S(2)}, u32[]{:S(2)}) collective-permute-start(bf16[128,512]{1,0:T(8,128)(2,1)S(1)} %select_convert_fusion.7), channel_id=1, source_target_pairs={{0,2},{2,0},{4,6},{6,4},{8,10},{10,8},{12,14},{14,12},{1,3},{3,1},... | collective-permute-start | bytes 393224 | tf_op jit(solution)/shard_map/ppermute | solution.py:18
  11.7 6.5 %collective-permute-start.16 = (bf16[128,256]{1,0:T(8,128)(2,1)S(1)}, bf16[128,256]{1,0:T(8,128)(2,1)S(1)}, u32[]{:S(2)}, u32[]{:S(2)}) collective-permute-start(bf16[128,256]{1,0:T(8,128)(2,1)S(1)} %select_convert_fusion.12), channel_id=1, source_target_pairs={{0,2},{2,0},{4,6},{6,4},{8,10},{10,8},{12,14},{14,12},{1,3},{3,1},... | collective-permute-start | bytes 196616 | tf_op jit(solution)/shard_map/ppermute | solution.py:18
  14.1 25.9 %copy-start.1 = (bf16[512,4096]{1,0:T(8,128)(2,1)S(1)}, bf16[512,4096]{1,0:T(8,128)(2,1)}, u32[]{:S(2)}) copy-start(bf16[512,4096]{1,0:T(8,128)(2,1)} %slab_ref.3) | copy-start | bytes 12582916
  14.1 6.7 %collective-permute-start.11 = (bf16[128,256]{1,0:T(8,128)(2,1)S(1)}, bf16[128,256]{1,0:T(8,128)(2,1)S(1)}, u32[]{:S(2)}, u32[]{:S(2)}) collective-permute-start(bf16[128,256]{1,0:T(8,128)(2,1)S(1)} %select_convert_fusion.13), channel_id=1, source_target_pairs={{0,4},{2,6},{4,0},{6,2},{8,12},{10,14},{12,8},{14,10},{1,5},{3,7},... | collective-permute-start | bytes 196616 | tf_op jit(solution)/shard_map/ppermute | solution.py:18
  15.9 5.8 %collective-permute-start.6 = (bf16[128,256]{1,0:T(8,128)(2,1)S(1)}, bf16[128,256]{1,0:T(8,128)(2,1)S(1)}, u32[]{:S(2)}, u32[]{:S(2)}) collective-permute-start(bf16[128,256]{1,0:T(8,128)(2,1)S(1)} %select_convert_fusion.14), channel_id=1, source_target_pairs={{0,2},{2,0},{4,6},{6,4},{8,10},{10,8},{12,14},{14,12},{1,3},{3,1},... | collective-permute-start | bytes 196616 | tf_op jit(solution)/shard_map/ppermute | solution.py:18
  16.7 7.3 %collective-permute-start.1 = (bf16[128,256]{1,0:T(8,128)(2,1)S(1)}, bf16[128,256]{1,0:T(8,128)(2,1)S(1)}, u32[]{:S(2)}, u32[]{:S(2)}) collective-permute-start(bf16[128,256]{1,0:T(8,128)(2,1)S(1)} %select_convert_fusion.15), channel_id=1, source_target_pairs={{0,4},{2,6},{4,0},{6,2},{8,12},{10,14},{12,8},{14,10},{1,5},{3,7},... | collective-permute-start | bytes 196616 | tf_op jit(solution)/shard_map/ppermute | solution.py:18
  18.2 8.8 %collective-permute-start.17 = (bf16[128,256]{1,0:T(8,128)(2,1)S(1)}, bf16[128,256]{1,0:T(8,128)(2,1)S(1)}, u32[]{:S(2)}, u32[]{:S(2)}) collective-permute-start(bf16[128,256]{1,0:T(8,128)(2,1)S(1)} %fusion.41), channel_id=1, source_target_pairs={{0,8},{2,10},{4,12},{6,14},{8,0},{10,2},{12,4},{14,6},{1,9},{3,11}... | collective-permute-start | bytes 196616 | tf_op jit(solution)/shard_map/ppermute | solution.py:18
  20.9 9.1 %collective-permute-start.12 = (bf16[128,256]{1,0:T(8,128)(2,1)S(1)}, bf16[128,256]{1,0:T(8,128)(2,1)S(1)}, u32[]{:S(2)}, u32[]{:S(2)}) collective-permute-start(bf16[128,256]{1,0:T(8,128)(2,1)S(1)} %fusion.40), channel_id=1, source_target_pairs={{0,8},{2,10},{4,12},{6,14},{8,0},{10,2},{12,4},{14,6},{1,9},{3,11}... | collective-permute-start | bytes 196616 | tf_op jit(solution)/shard_map/ppermute | solution.py:18
  21.8 9.3 %collective-permute-start.7 = (bf16[128,256]{1,0:T(8,128)(2,1)S(1)}, bf16[128,256]{1,0:T(8,128)(2,1)S(1)}, u32[]{:S(2)}, u32[]{:S(2)}) collective-permute-start(bf16[128,256]{1,0:T(8,128)(2,1)S(1)} %fusion.39), channel_id=1, source_target_pairs={{0,8},{2,10},{4,12},{6,14},{8,0},{10,2},{12,4},{14,6},{1,9},{3,11}... | collective-permute-start | bytes 196616 | tf_op jit(solution)/shard_map/ppermute | solution.py:18
  24.0 8.3 %collective-permute-start.2 = (bf16[128,256]{1,0:T(8,128)(2,1)S(1)}, bf16[128,256]{1,0:T(8,128)(2,1)S(1)}, u32[]{:S(2)}, u32[]{:S(2)}) collective-permute-start(bf16[128,256]{1,0:T(8,128)(2,1)S(1)} %fusion.38), channel_id=1, source_target_pairs={{0,8},{2,10},{4,12},{6,14},{8,0},{10,2},{12,4},{14,6},{1,9},{3,11}... | collective-permute-start | bytes 196616 | tf_op jit(solution)/shard_map/ppermute | solution.py:18
  27.1 6.4 %collective-permute-start.18 = (bf16[128,256]{1,0:T(8,128)(2,1)S(1)}, bf16[128,256]{1,0:T(8,128)(2,1)S(1)}, u32[]{:S(2)}, u32[]{:S(2)}) collective-permute-start(bf16[128,256]{1,0:T(8,128)(2,1)S(1)} %multiply_convert_fusion), channel_id=1, source_target_pairs={{0,2},{2,0},{4,6},{6,4},{8,10},{10,8},{12,14},{14,12},{1,3},{3,1},... | collective-permute-start | bytes 196616 | tf_op jit(solution)/shard_map/ppermute | solution.py:18
  30.0 5.0 %collective-permute-start.13 = (bf16[128,256]{1,0:T(8,128)(2,1)S(1)}, bf16[128,256]{1,0:T(8,128)(2,1)S(1)}, u32[]{:S(2)}, u32[]{:S(2)}) collective-permute-start(bf16[128,256]{1,0:T(8,128)(2,1)S(1)} %multiply_convert_fusion.1), channel_id=1, source_target_pairs={{0,4},{2,6},{4,0},{6,2},{8,12},{10,14},{12,8},{14,10},{1,5},{3,7},... | collective-permute-start | bytes 196616 | tf_op jit(solution)/shard_map/ppermute | solution.py:18
  31.1 5.1 %collective-permute-start.8 = (bf16[128,256]{1,0:T(8,128)(2,1)S(1)}, bf16[128,256]{1,0:T(8,128)(2,1)S(1)}, u32[]{:S(2)}, u32[]{:S(2)}) collective-permute-start(bf16[128,256]{1,0:T(8,128)(2,1)S(1)} %multiply_convert_fusion.2), channel_id=1, source_target_pairs={{0,2},{2,0},{4,6},{6,4},{8,10},{10,8},{12,14},{14,12},{1,3},{3,1},... | collective-permute-start | bytes 196616 | tf_op jit(solution)/shard_map/ppermute | solution.py:18
  32.3 5.1 %collective-permute-start.3 = (bf16[128,256]{1,0:T(8,128)(2,1)S(1)}, bf16[128,256]{1,0:T(8,128)(2,1)S(1)}, u32[]{:S(2)}, u32[]{:S(2)}) collective-permute-start(bf16[128,256]{1,0:T(8,128)(2,1)S(1)} %multiply_convert_fusion.3), channel_id=1, source_target_pairs={{0,4},{2,6},{4,0},{6,2},{8,12},{10,14},{12,8},{14,10},{1,5},{3,7},... | collective-permute-start | bytes 196616 | tf_op jit(solution)/shard_map/ppermute | solution.py:18
  33.5 6.4 %collective-permute-start.19 = (bf16[128,512]{1,0:T(8,128)(2,1)S(1)}, bf16[128,512]{1,0:T(8,128)(2,1)S(1)}, u32[]{:S(2)}, u32[]{:S(2)}) collective-permute-start(bf16[128,512]{1,0:T(8,128)(2,1)S(1)} %pad_maximum_fusion.4), channel_id=1, source_target_pairs={{0,4},{2,6},{4,0},{6,2},{8,12},{10,14},{12,8},{14,10},{1,5},{3,7},... | collective-permute-start | bytes 393224 | tf_op jit(solution)/shard_map/ppermute | solution.py:18
  35.0 5.6 %collective-permute-start.14 = (bf16[128,512]{1,0:T(8,128)(2,1)S(1)}, bf16[128,512]{1,0:T(8,128)(2,1)S(1)}, u32[]{:S(2)}, u32[]{:S(2)}) collective-permute-start(bf16[128,512]{1,0:T(8,128)(2,1)S(1)} %pad_maximum_fusion.3), channel_id=1, source_target_pairs={{0,2},{2,0},{4,6},{6,4},{8,10},{10,8},{12,14},{14,12},{1,3},{3,1},... | collective-permute-start | bytes 393224 | tf_op jit(solution)/shard_map/ppermute | solution.py:18
  36.3 5.0 %collective-permute-start.9 = (bf16[128,512]{1,0:T(8,128)(2,1)S(1)}, bf16[128,512]{1,0:T(8,128)(2,1)S(1)}, u32[]{:S(2)}, u32[]{:S(2)}) collective-permute-start(bf16[128,512]{1,0:T(8,128)(2,1)S(1)} %pad_maximum_fusion.2), channel_id=1, source_target_pairs={{0,4},{2,6},{4,0},{6,2},{8,12},{10,14},{12,8},{14,10},{1,5},{3,7},... | collective-permute-start | bytes 393224 | tf_op jit(solution)/shard_map/ppermute | solution.py:18
  37.5 5.0 %collective-permute-start.4 = (bf16[128,512]{1,0:T(8,128)(2,1)S(1)}, bf16[128,512]{1,0:T(8,128)(2,1)S(1)}, u32[]{:S(2)}, u32[]{:S(2)}) collective-permute-start(bf16[128,512]{1,0:T(8,128)(2,1)S(1)} %pad_maximum_fusion.1), channel_id=1, source_target_pairs={{0,2},{2,0},{4,6},{6,4},{8,10},{10,8},{12,14},{14,12},{1,3},{3,1},... | collective-permute-start | bytes 393224 | tf_op jit(solution)/shard_map/ppermute | solution.py:18
  43.0 1.6 %collective-permute-start.20 = (f32[512,128]{1,0:T(8,128)S(1)}, f32[512,128]{1,0:T(8,128)S(1)}, u32[]{:S(2)}, u32[]{:S(2)}) collective-permute-start(f32[512,128]{1,0:T(8,128)S(1)} %fusion.2.mine_ref), channel_id=1, source_target_pairs={{0,1},{1,0},{2,3},{3,2},{4,5},{5,4},{6,7},{7,6},{8,9},{9,8},{10,11... | collective-permute-start | bytes 786440 | tf_op jit(solution)/shard_map/ppermute | solution.py:18
  45.1 6.8 %collective-permute-start.24 = (f32[72,128]{1,0:T(8,128)S(1)}, f32[72,128]{1,0:T(8,128)S(1)}, u32[]{:S(2)}, u32[]{:S(2)}) collective-permute-start(f32[72,128]{1,0:T(8,128)S(1)} %make_gram.1), channel_id=1, source_target_pairs={{0,10},{1,15},{2,8},{3,13},{4,14},{5,11},{6,12},{7,9},{8,2},{9,7},... | collective-permute-start | bytes 110600 | tf_op jit(solution)/shard_map/ppermute | solution.py:36
  47.1 5.6 %collective-permute-start.23 = (f32[72,128]{1,0:T(8,128)S(1)}, f32[72,128]{1,0:T(8,128)S(1)}, u32[]{:S(2)}, u32[]{:S(2)}) collective-permute-start(f32[72,128]{1,0:T(8,128)S(1)} %make_gram.1), channel_id=1, source_target_pairs={{0,8},{1,13},{2,10},{3,15},{4,12},{5,9},{6,14},{7,11},{8,0},{9,5},... | collective-permute-start | bytes 110600 | tf_op jit(solution)/shard_map/ppermute | solution.py:36
  48.5 4.2 %collective-permute-start.22 = (f32[72,128]{1,0:T(8,128)S(1)}, f32[72,128]{1,0:T(8,128)S(1)}, u32[]{:S(2)}, u32[]{:S(2)}) collective-permute-start(f32[72,128]{1,0:T(8,128)S(1)} %make_gram.1), channel_id=1, source_target_pairs={{0,2},{1,7},{2,0},{3,5},{4,6},{5,3},{6,4},{7,1},{8,10},{9,15},{10,... | collective-permute-start | bytes 110600 | tf_op jit(solution)/shard_map/ppermute | solution.py:36
  49.5 3.1 %collective-permute-start.21 = (f32[72,128]{1,0:T(8,128)S(1)}, f32[72,128]{1,0:T(8,128)S(1)}, u32[]{:S(2)}, u32[]{:S(2)}) collective-permute-start(f32[72,128]{1,0:T(8,128)S(1)} %make_gram.1), channel_id=1, source_target_pairs={{1,5},{3,7},{5,1},{7,3},{9,13},{11,15},{13,9},{15,11},{17,21},{19,... | collective-permute-start | bytes 110600 | tf_op jit(solution)/shard_map/ppermute | solution.py:36
  52.7 2.4 %collective-permute-start.25 = (f32[72,128]{1,0:T(8,128)S(1)}, f32[72,128]{1,0:T(8,128)S(1)}, u32[]{:S(2)}, u32[]{:S(2)}) collective-permute-start(f32[72,128]{1,0:T(8,128)S(1)} %add_add_fusion), channel_id=1, source_target_pairs={{0,1},{1,0},{2,3},{3,2},{4,5},{5,4},{6,7},{7,6},{8,9},{9,8},{10,11... | collective-permute-start | bytes 110600 | tf_op jit(solution)/shard_map/ppermute | solution.py:18
  59.8 6.1 %collective-permute-start.26 = (bf16[2,2,16,1024]{3,2,0,1:T(8,128)(2,1)S(1)}, bf16[2,2,16,1024]{3,2,0,1:T(8,128)(2,1)S(1)}, u32[]{:S(2)}, u32[]{:S(2)}) collective-permute-start(bf16[2,2,16,1024]{3,2,0,1:T(8,128)(2,1)S(1)} %fusion.22), channel_id=1, source_target_pairs={{0,2},{2,0},{4,6},{6,4},{8,10},{10,8},{12,14},{14,12},{1,3},{3,1},... | collective-permute-start | bytes 393224 | tf_op jit(solution)/shard_map/ppermute | solution.py:18
  61.0 7.1 %collective-permute-start.29 = (bf16[2,2,16,1024]{3,2,0,1:T(8,128)(2,1)S(1)}, bf16[2,2,16,1024]{3,2,0,1:T(8,128)(2,1)S(1)}, u32[]{:S(2)}, u32[]{:S(2)}) collective-permute-start(bf16[2,2,16,1024]{3,2,0,1:T(8,128)(2,1)S(1)} %fusion.23), channel_id=1, source_target_pairs={{0,4},{2,6},{4,0},{6,2},{8,12},{10,14},{12,8},{14,10},{1,5},{3,7},... | collective-permute-start | bytes 393224 | tf_op jit(solution)/shard_map/ppermute | solution.py:18
  62.8 6.4 %collective-permute-start.32 = (bf16[2,2,16,1024]{3,2,0,1:T(8,128)(2,1)S(1)}, bf16[2,2,16,1024]{3,2,0,1:T(8,128)(2,1)S(1)}, u32[]{:S(2)}, u32[]{:S(2)}) collective-permute-start(bf16[2,2,16,1024]{3,2,0,1:T(8,128)(2,1)S(1)} %fusion.24), channel_id=1, source_target_pairs={{0,2},{2,0},{4,6},{6,4},{8,10},{10,8},{12,14},{14,12},{1,3},{3,1},... | collective-permute-start | bytes 393224 | tf_op jit(solution)/shard_map/ppermute | solution.py:18
  64.0 6.4 %collective-permute-start.35 = (bf16[2,2,16,1024]{3,2,0,1:T(8,128)(2,1)S(1)}, bf16[2,2,16,1024]{3,2,0,1:T(8,128)(2,1)S(1)}, u32[]{:S(2)}, u32[]{:S(2)}) collective-permute-start(bf16[2,2,16,1024]{3,2,0,1:T(8,128)(2,1)S(1)} %fusion.25), channel_id=1, source_target_pairs={{0,4},{2,6},{4,0},{6,2},{8,12},{10,14},{12,8},{14,10},{1,5},{3,7},... | collective-permute-start | bytes 393224 | tf_op jit(solution)/shard_map/ppermute | solution.py:18
  66.0 5.6 %collective-permute-start.27 = (bf16[2,16,1024]{2,1,0:T(8,128)(2,1)S(1)}, bf16[2,16,1024]{2,1,0:T(8,128)(2,1)S(1)}, u32[]{:S(2)}, u32[]{:S(2)}) collective-permute-start(bf16[2,16,1024]{2,1,0:T(8,128)(2,1)S(1)} %fusion.26), channel_id=1, source_target_pairs={{0,4},{2,6},{4,0},{6,2},{8,12},{10,14},{12,8},{14,10},{1,5},{3,7},... | collective-permute-start | bytes 196616 | tf_op jit(solution)/shard_map/ppermute | solution.py:18
  68.2 5.3 %collective-permute-start.30 = (bf16[2,16,1024]{2,1,0:T(8,128)(2,1)S(1)}, bf16[2,16,1024]{2,1,0:T(8,128)(2,1)S(1)}, u32[]{:S(2)}, u32[]{:S(2)}) collective-permute-start(bf16[2,16,1024]{2,1,0:T(8,128)(2,1)S(1)} %fusion.27), channel_id=1, source_target_pairs={{0,2},{2,0},{4,6},{6,4},{8,10},{10,8},{12,14},{14,12},{1,3},{3,1},... | collective-permute-start | bytes 196616 | tf_op jit(solution)/shard_map/ppermute | solution.py:18
  69.3 5.4 %collective-permute-start.33 = (bf16[2,16,1024]{2,1,0:T(8,128)(2,1)S(1)}, bf16[2,16,1024]{2,1,0:T(8,128)(2,1)S(1)}, u32[]{:S(2)}, u32[]{:S(2)}) collective-permute-start(bf16[2,16,1024]{2,1,0:T(8,128)(2,1)S(1)} %fusion.28), channel_id=1, source_target_pairs={{0,4},{2,6},{4,0},{6,2},{8,12},{10,14},{12,8},{14,10},{1,5},{3,7},... | collective-permute-start | bytes 196616 | tf_op jit(solution)/shard_map/ppermute | solution.py:18
  70.5 6.1 %collective-permute-start.36 = (bf16[2,16,1024]{2,1,0:T(8,128)(2,1)S(1)}, bf16[2,16,1024]{2,1,0:T(8,128)(2,1)S(1)}, u32[]{:S(2)}, u32[]{:S(2)}) collective-permute-start(bf16[2,16,1024]{2,1,0:T(8,128)(2,1)S(1)} %fusion.29), channel_id=1, source_target_pairs={{0,2},{2,0},{4,6},{6,4},{8,10},{10,8},{12,14},{14,12},{1,3},{3,1},... | collective-permute-start | bytes 196616 | tf_op jit(solution)/shard_map/ppermute | solution.py:18
  71.6 6.3 %collective-permute-start.28 = (bf16[16,1024]{1,0:T(8,128)(2,1)S(1)}, bf16[16,1024]{1,0:T(8,128)(2,1)S(1)}, u32[]{:S(2)}, u32[]{:S(2)}) collective-permute-start(bf16[16,1024]{1,0:T(8,128)(2,1)S(1)} %fusion.34), channel_id=1, source_target_pairs={{0,8},{2,10},{4,12},{6,14},{8,0},{10,2},{12,4},{14,6},{1,9},{3,11}... | collective-permute-start | bytes 98312 | tf_op jit(solution)/shard_map/ppermute | solution.py:18
  73.5 5.8 %collective-permute-start.31 = (bf16[16,1024]{1,0:T(8,128)(2,1)S(1)}, bf16[16,1024]{1,0:T(8,128)(2,1)S(1)}, u32[]{:S(2)}, u32[]{:S(2)}) collective-permute-start(bf16[16,1024]{1,0:T(8,128)(2,1)S(1)} %fusion.35), channel_id=1, source_target_pairs={{0,8},{2,10},{4,12},{6,14},{8,0},{10,2},{12,4},{14,6},{1,9},{3,11}... | collective-permute-start | bytes 98312 | tf_op jit(solution)/shard_map/ppermute | solution.py:18
  74.8 4.9 %collective-permute-start.34 = (bf16[16,1024]{1,0:T(8,128)(2,1)S(1)}, bf16[16,1024]{1,0:T(8,128)(2,1)S(1)}, u32[]{:S(2)}, u32[]{:S(2)}) collective-permute-start(bf16[16,1024]{1,0:T(8,128)(2,1)S(1)} %fusion.36), channel_id=1, source_target_pairs={{0,8},{2,10},{4,12},{6,14},{8,0},{10,2},{12,4},{14,6},{1,9},{3,11}... | collective-permute-start | bytes 98312 | tf_op jit(solution)/shard_map/ppermute | solution.py:18
  76.7 5.2 %collective-permute-start.37 = (bf16[16,1024]{1,0:T(8,128)(2,1)S(1)}, bf16[16,1024]{1,0:T(8,128)(2,1)S(1)}, u32[]{:S(2)}, u32[]{:S(2)}) collective-permute-start(bf16[16,1024]{1,0:T(8,128)(2,1)S(1)} %fusion.37), channel_id=1, source_target_pairs={{0,8},{2,10},{4,12},{6,14},{8,0},{10,2},{12,4},{14,6},{1,9},{3,11}... | collective-permute-start | bytes 98312 | tf_op jit(solution)/shard_map/ppermute | solution.py:18

commit v16 on v15

--- a/solution.py
+++ b/solution.py
@@ -42,19 +42,61 @@
     return value
 
 
-def scatter_sum(value, axis, order):
-    rows, cols = value.shape[0] >> len(order), value.shape[1]
-    total = value.reshape([2] * len(order) + [rows, cols])
-    left = sorted(order, reverse=True)
-    for bit in order:
-        dim = left.index(bit)
-        left.remove(bit)
-        low = lax.index_in_dim(total, 0, dim, keepdims=False)
-        high = lax.index_in_dim(total, 1, dim, keepdims=False)
-        upper = bit_of(axis, bit) == 1
-        send = jnp.where(upper, low, high).astype(jnp.bfloat16)
-        landed = swap(send, axis, 1 << bit)
-        total = jnp.where(upper, high, low) + landed.astype(jnp.float32)
+def levels_of(size):
+    levels, stride = [], 1
+    while stride < size:
+        radix = 2 if stride == 1 else min(4, size // stride)
+        levels.append((stride, radix))
+        stride *= radix
+    return levels
+
+
+def own_block(total, axis, stride, radix, dim):
+    digit = lax.rem(lax.div(lax.axis_index(axis), stride), radix)
+    return lax.dynamic_slice_in_dim(total, digit, 1, dim)
+
+
+def sent_blocks(total, axis, stride, radix, dim):
+    digit = lax.rem(lax.div(lax.axis_index(axis), stride), radix)
+    return [
+        lax.dynamic_slice_in_dim(total, jnp.bitwise_xor(digit, t), 1, dim).astype(jnp.bfloat16)
+        for t in range(1, radix)
+    ]
+
+
+def after(value, *others):
+    return lax.optimization_barrier((value, others))[0]
+
+
+def scatter_sums(values, axis):
+    levels = levels_of(lax.axis_size(axis))
+    shape = [radix for _, radix in reversed(levels)]
+    rows = values[0].shape[0] // lax.axis_size(axis)
+    totals = [value.reshape(shape + [rows, value.shape[1]]) for value in values]
+    orders = [list(range(len(levels))), list(range(len(levels)))[::-1]]
+    landed = [[], []]
+    for step in range(len(levels)):
+        for which in range(2):
+            level = orders[which][step]
+            stride, radix = levels[level]
+            dim = len(levels) - 1 - level
+            total = add_terms(totals[which], landed[which])
+            sends = sent_blocks(total, axis, stride, radix, dim)
+            if step:
+                landed[1 - which] = after(landed[1 - which], sends)
+            elif which == 0:
+                totals[1] = after(totals[1], sends)
+            landed[which] = [swap(send, axis, t * stride) for t, send in enumerate(sends, 1)]
+            totals[which] = own_block(total, axis, stride, radix, dim)
+    return [
+        add_terms(total, terms).reshape(rows, total.shape[-1])
+        for total, terms in zip(totals, landed)
+    ]
+
+
+def add_terms(total, terms):
+    for term in terms:
+        total = total + term.astype(jnp.float32)
     return total
 
 
@@ -268,20 +310,21 @@
             (((1,), (0,)), ((), ())),
             preferred_element_type=jnp.float32,
         )
-        out, inner = divmod(start, products[0].shape[1])
+        out = 0 if start < products[0].shape[1] else 1
+        inner = start - out * products[0].shape[1]
         products[out][:, inner : inner + TILE] = both[:width] + both[width:]
 
 
-def make_basis(gram, mine, other, slab, total_cols, root_rows, chunks):
+def make_basis(gram, mine, other, slab, total_cols, root_rows, cut):
     rows, width = mine.shape
     cols = slab.shape[1]
     return pl.pallas_call(
         functools.partial(basis_kernel, total_cols, root_rows),
         out_shape=[jax.ShapeDtypeStruct((rows, width), jnp.float32)]
-        + [jax.ShapeDtypeStruct((width, cols // chunks), jnp.float32)] * chunks,
+        + [jax.ShapeDtypeStruct((width, part), jnp.float32) for part in (cut, cols - cut)],
         in_specs=[pl.BlockSpec(memory_space=pltpu.VMEM)] * 3
         + [pl.BlockSpec(memory_space=pl.ANY)],
-        out_specs=[pl.BlockSpec(memory_space=pltpu.VMEM)] * (1 + chunks),
+        out_specs=[pl.BlockSpec(memory_space=pltpu.VMEM)] * 3,
         scratch_shapes=[
             pltpu.VMEM((width, width), jnp.float32),
             pltpu.VMEM((width, width), jnp.float32),
@@ -316,14 +359,12 @@
         )
     other_sketch = swap(partial_sketch, "col", 1)
     gram = row_sum(make_gram(partial_sketch, other_sketch, total_cols))
+    cut = cols_here * 5 // 8
     basis, *products = make_basis(
-        gram, partial_sketch, other_sketch, activations, total_cols, root_rows, CHUNKS
+        gram, partial_sketch, other_sketch, activations, total_cols, root_rows, cut
     )
 
-    pieces = [
-        scatter_sum(product, "row", orders[c % 2]) / total_rows
-        for c, product in enumerate(products)
-    ]
+    pieces = [total / total_rows for total in scatter_sums(products, "row")]
     return (basis, jnp.concatenate(pieces, axis=1))
 
 

time: 82.8 us -> 84.1 us (1.016)
  waiting for transfers between devices: 19.5 us -> 26.1 us
  starting transfers between devices: 49 us -> 44.2 us
    ppermute x34 -> x30, waiting for transfers between devices: 17 us -> 23.6 us  [swap(): return lax.ppermute(value, axis, [(i, i ^ distance) for i in range(size)])]
    ppermute x34 -> x30, starting transfers between devices: 43.9 us -> 39.1 us  [swap(): return lax.ppermute(value, axis, [(i, i ^ distance) for i in range(size)])]
  transfers between devices with their start and end apart: 38 -> 34, of which waited for: 18 -> 18; matrix products, arithmetic and copies ran while one was open for 3% -> 3% of each run, Pallas kernels for 0% -> 0%
where the time goes in v16:
time: 84.1 us; the launch traced here: 84 us
  starting transfers between devices  44.2 us (53%)
  waiting for transfers between devices  26.1 us (31%)
  Pallas kernels  8.12 us (10%)
  other arithmetic  1.78 us (2%)
  matrix products  1.74 us (2%)
  local copies, waits for them, and re-layouts  1.03 us (1%)
  between operations  0.99 us (1%)
    ppermute x30, starting transfers between devices, swap(): return lax.ppermute(value, axis, [(i, i ^ distance) for i in range(size)])  39.1 us
    ppermute x30, waiting for transfers between devices, swap(): return lax.ppermute(value, axis, [(i, i ^ distance) for i in range(size)])  23.6 us
    ppermute x4, starting transfers between devices, row_sum(): terms.append(lax.ppermute(value, ('row', 'col'), pairs))  5.1 us
    pallas_call x1, Pallas kernels, make_basis(): pl.pallas_call(functools.partial(basis_kernel, total_cols, root_rows), ou...  4.63 us
    pallas_call x1, Pallas kernels, first_product(): pl.pallas_call(sketch_kernel, out_shape=[jax.ShapeDtypeStruct((width, col...  3 us
    ppermute x4, waiting for transfers between devices, row_sum(): terms.append(lax.ppermute(value, ('row', 'col'), pairs))  2.51 us
    dot_general x4, matrix products, per_device(): lax.dot_general(activations[:, span], shared, (((1,), (1,)), ((), ())), p...  1.74 us
  transfers between devices with their start and end apart: 34, of which 18 were waited for; matrix products, arithmetic and copies ran while one was open for 3% of the time, Pallas kernels for 0%

profile of v16, /device:TPU:0, one launch (start us, length us, event | category | flops | bytes accessed | tf_op | source)
XLA Modules:
  0.0 84.0 jit_solution(14039042245214221492)
XLA Ops:
  0.7 0.9 %copy-done = bf16[512,128]{1,0:T(8,128)(2,1)S(1)} copy-done((bf16[512,128]{1,0:T(8,128)(2,1)S(1)}, bf16[512,128]{1,0:T(8,128)(2,1)}, u32[]{:S(2)}) %copy-start) | copy-done | bytes 131096
  1.6 3.0 %first_product.1 = (f32[128,1024]{1,0:T(8,128)S(1)}, f32[128,1024]{1,0:T(8,128)S(1)}, f32[128,1024]{1,0:T(8,128)S(1)}, f32[128,1024]{1,0:T(8,128)S(1)}) custom-call(bf16[512,128]{1,0:T(8,128)(2,1)S(1)} %copy-done, bf16[512,4096]{1,0:T(8,128)(2,1)} %slab_ref.3), custom_call_target="tpu_custom_call" | custom-call | flops 536870912 | bytes 4194304 | tf_op jit(solution)/shard_map/first_product/pallas_call | solution.py:160
  4.6 3.1 %collective-permute-start.15 = (bf16[128,512]{1,0:T(8,128)(2,1)S(1)}, bf16[128,512]{1,0:T(8,128)(2,1)S(1)}, u32[]{:S(2)}, u32[]{:S(2)}) collective-permute-start(bf16[128,512]{1,0:T(8,128)(2,1)S(1)} %select_convert_fusion), channel_id=1, source_target_pairs={{0,4},{2,6},{4,0},{6,2},{8,12},{10,14},{12,8},{14,10},{1,5},{3,7},... | collective-permute-start | bytes 393224 | tf_op jit(solution)/shard_map/ppermute | solution.py:18
  7.7 1.6 %collective-permute-start.10 = (bf16[128,512]{1,0:T(8,128)(2,1)S(1)}, bf16[128,512]{1,0:T(8,128)(2,1)S(1)}, u32[]{:S(2)}, u32[]{:S(2)}) collective-permute-start(bf16[128,512]{1,0:T(8,128)(2,1)S(1)} %select_convert_fusion.1), channel_id=1, source_target_pairs={{0,2},{2,0},{4,6},{6,4},{8,10},{10,8},{12,14},{14,12},{1,3},{3,1},... | collective-permute-start | bytes 393224 | tf_op jit(solution)/shard_map/ppermute | solution.py:18
  9.3 0.5 collective-permute-start.5
  10.0 1.6 %collective-permute-done.15 = bf16[128,512]{1,0:T(8,128)(2,1)S(1)} collective-permute-done((bf16[128,512]{1,0:T(8,128)(2,1)S(1)}, bf16[128,512]{1,0:T(8,128)(2,1)S(1)}, u32[]{:S(2)}, u32[]{:S(2)}) %collective-permute-start.15) | collective-permute-done | bytes 131104 | tf_op jit(solution)/shard_map/ppermute | solution.py:18
  11.7 2.4 %collective-permute-start.16 = (bf16[128,256]{1,0:T(8,128)(2,1)S(1)}, bf16[128,256]{1,0:T(8,128)(2,1)S(1)}, u32[]{:S(2)}, u32[]{:S(2)}) collective-permute-start(bf16[128,256]{1,0:T(8,128)(2,1)S(1)} %select_convert_fusion.4), channel_id=1, source_target_pairs={{0,2},{2,0},{4,6},{6,4},{8,10},{10,8},{12,14},{14,12},{1,3},{3,1},... | collective-permute-start | bytes 196616 | tf_op jit(solution)/shard_map/ppermute | solution.py:18
  14.1 1.7 %collective-permute-start.11 = (bf16[128,256]{1,0:T(8,128)(2,1)S(1)}, bf16[128,256]{1,0:T(8,128)(2,1)S(1)}, u32[]{:S(2)}, u32[]{:S(2)}) collective-permute-start(bf16[128,256]{1,0:T(8,128)(2,1)S(1)} %select_convert_fusion.5), channel_id=1, source_target_pairs={{0,4},{2,6},{4,0},{6,2},{8,12},{10,14},{12,8},{14,10},{1,5},{3,7},... | collective-permute-start | bytes 196616 | tf_op jit(solution)/shard_map/ppermute | solution.py:18
  16.0 0.6 collective-permute-start.6
  16.7 1.5 %collective-permute-start.1 = (bf16[128,256]{1,0:T(8,128)(2,1)S(1)}, bf16[128,256]{1,0:T(8,128)(2,1)S(1)}, u32[]{:S(2)}, u32[]{:S(2)}) collective-permute-start(bf16[128,256]{1,0:T(8,128)(2,1)S(1)} %select_convert_fusion.7), channel_id=1, source_target_pairs={{0,4},{2,6},{4,0},{6,2},{8,12},{10,14},{12,8},{14,10},{1,5},{3,7},... | collective-permute-start | bytes 196616 | tf_op jit(solution)/shard_map/ppermute | solution.py:18
  18.2 2.6 %collective-permute-start.17 = (bf16[128,256]{1,0:T(8,128)(2,1)S(1)}, bf16[128,256]{1,0:T(8,128)(2,1)S(1)}, u32[]{:S(2)}, u32[]{:S(2)}) collective-permute-start(bf16[128,256]{1,0:T(8,128)(2,1)S(1)} %fusion.25), channel_id=1, source_target_pairs={{0,8},{2,10},{4,12},{6,14},{8,0},{10,2},{12,4},{14,6},{1,9},{3,11}... | collective-permute-start | bytes 196616 | tf_op jit(solution)/shard_map/ppermute | solution.py:18
  20.9 0.9 %collective-permute-start.12 = (bf16[128,256]{1,0:T(8,128)(2,1)S(1)}, bf16[128,256]{1,0:T(8,128)(2,1)S(1)}, u32[]{:S(2)}, u32[]{:S(2)}) collective-permute-start(bf16[128,256]{1,0:T(8,128)(2,1)S(1)} %fusion.24), channel_id=1, source_target_pairs={{0,8},{2,10},{4,12},{6,14},{8,0},{10,2},{12,4},{14,6},{1,9},{3,11}... | collective-permute-start | bytes 196616 | tf_op jit(solution)/shard_map/ppermute | solution.py:18
  21.8 2.2 %collective-permute-start.7 = (bf16[128,256]{1,0:T(8,128)(2,1)S(1)}, bf16[128,256]{1,0:T(8,128)(2,1)S(1)}, u32[]{:S(2)}, u32[]{:S(2)}) collective-permute-start(bf16[128,256]{1,0:T(8,128)(2,1)S(1)} %fusion.23), channel_id=1, source_target_pairs={{0,8},{2,10},{4,12},{6,14},{8,0},{10,2},{12,4},{14,6},{1,9},{3,11}... | collective-permute-start | bytes 196616 | tf_op jit(solution)/shard_map/ppermute | solution.py:18
  24.0 0.9 %collective-permute-start.2 = (bf16[128,256]{1,0:T(8,128)(2,1)S(1)}, bf16[128,256]{1,0:T(8,128)(2,1)S(1)}, u32[]{:S(2)}, u32[]{:S(2)}) collective-permute-start(bf16[128,256]{1,0:T(8,128)(2,1)S(1)} %fusion.22), channel_id=1, source_target_pairs={{0,8},{2,10},{4,12},{6,14},{8,0},{10,2},{12,4},{14,6},{1,9},{3,11}... | collective-permute-start | bytes 196616 | tf_op jit(solution)/shard_map/ppermute | solution.py:18
  24.9 2.2 %collective-permute-done.17 = bf16[128,256]{1,0:T(8,128)(2,1)S(1)} collective-permute-done((bf16[128,256]{1,0:T(8,128)(2,1)S(1)}, bf16[128,256]{1,0:T(8,128)(2,1)S(1)}, u32[]{:S(2)}, u32[]{:S(2)}) %collective-permute-start.17) | collective-permute-done | bytes 65568 | tf_op jit(solution)/shard_map/ppermute | solution.py:18
  27.1 1.8 %collective-permute-start.18 = (bf16[128,256]{1,0:T(8,128)(2,1)S(1)}, bf16[128,256]{1,0:T(8,128)(2,1)S(1)}, u32[]{:S(2)}, u32[]{:S(2)}) collective-permute-start(bf16[128,256]{1,0:T(8,128)(2,1)S(1)} %multiply_convert_fusion), channel_id=1, source_target_pairs={{0,2},{2,0},{4,6},{6,4},{8,10},{10,8},{12,14},{14,12},{1,3},{3,1},... | collective-permute-start | bytes 196616 | tf_op jit(solution)/shard_map/ppermute | solution.py:18
  28.9 1.1 %collective-permute-done.12 = bf16[128,256]{1,0:T(8,128)(2,1)S(1)} collective-permute-done((bf16[128,256]{1,0:T(8,128)(2,1)S(1)}, bf16[128,256]{1,0:T(8,128)(2,1)S(1)}, u32[]{:S(2)}, u32[]{:S(2)}) %collective-permute-start.12) | collective-permute-done | bytes 65568 | tf_op jit(solution)/shard_map/ppermute | solution.py:18
  30.1 1.0 %collective-permute-done.7 = bf16[128,256]{1,0:T(8,128)(2,1)S(1)} collective-permute-done((bf16[128,256]{1,0:T(8,128)(2,1)S(1)}, bf16[128,256]{1,0:T(8,128)(2,1)S(1)}, u32[]{:S(2)}, u32[]{:S(2)}) %collective-permute-start.7) | collective-permute-done | bytes 65568 | tf_op jit(solution)/shard_map/ppermute | solution.py:18
  31.1 1.2 %collective-permute-start.8 = (bf16[128,256]{1,0:T(8,128)(2,1)S(1)}, bf16[128,256]{1,0:T(8,128)(2,1)S(1)}, u32[]{:S(2)}, u32[]{:S(2)}) collective-permute-start(bf16[128,256]{1,0:T(8,128)(2,1)S(1)} %multiply_convert_fusion.2), channel_id=1, source_target_pairs={{0,2},{2,0},{4,6},{6,4},{8,10},{10,8},{12,14},{14,12},{1,3},{3,1},... | collective-permute-start | bytes 196616 | tf_op jit(solution)/shard_map/ppermute | solution.py:18
  32.3 1.1 %collective-permute-start.3 = (bf16[128,256]{1,0:T(8,128)(2,1)S(1)}, bf16[128,256]{1,0:T(8,128)(2,1)S(1)}, u32[]{:S(2)}, u32[]{:S(2)}) collective-permute-start(bf16[128,256]{1,0:T(8,128)(2,1)S(1)} %multiply_convert_fusion.3), channel_id=1, source_target_pairs={{0,4},{2,6},{4,0},{6,2},{8,12},{10,14},{12,8},{14,10},{1,5},{3,7},... | collective-permute-start | bytes 196616 | tf_op jit(solution)/shard_map/ppermute | solution.py:18
  33.5 1.0 %collective-permute-start.19 = (bf16[128,512]{1,0:T(8,128)(2,1)S(1)}, bf16[128,512]{1,0:T(8,128)(2,1)S(1)}, u32[]{:S(2)}, u32[]{:S(2)}) collective-permute-start(bf16[128,512]{1,0:T(8,128)(2,1)S(1)} %pad_maximum_fusion.4), channel_id=1, source_target_pairs={{0,4},{2,6},{4,0},{6,2},{8,12},{10,14},{12,8},{14,10},{1,5},{3,7},... | collective-permute-start | bytes 393224 | tf_op jit(solution)/shard_map/ppermute | solution.py:18
  35.1 1.2 %collective-permute-start.14 = (bf16[128,512]{1,0:T(8,128)(2,1)S(1)}, bf16[128,512]{1,0:T(8,128)(2,1)S(1)}, u32[]{:S(2)}, u32[]{:S(2)}) collective-permute-start(bf16[128,512]{1,0:T(8,128)(2,1)S(1)} %pad_maximum_fusion.3), channel_id=1, source_target_pairs={{0,2},{2,0},{4,6},{6,4},{8,10},{10,8},{12,14},{14,12},{1,3},{3,1},... | collective-permute-start | bytes 393224 | tf_op jit(solution)/shard_map/ppermute | solution.py:18
  36.3 0.9 %collective-permute-start.9 = (bf16[128,512]{1,0:T(8,128)(2,1)S(1)}, bf16[128,512]{1,0:T(8,128)(2,1)S(1)}, u32[]{:S(2)}, u32[]{:S(2)}) collective-permute-start(bf16[128,512]{1,0:T(8,128)(2,1)S(1)} %pad_maximum_fusion.2), channel_id=1, source_target_pairs={{0,4},{2,6},{4,0},{6,2},{8,12},{10,14},{12,8},{14,10},{1,5},{3,7},... | collective-permute-start | bytes 393224 | tf_op jit(solution)/shard_map/ppermute | solution.py:18
  37.5 1.1 %collective-permute-start.4 = (bf16[128,512]{1,0:T(8,128)(2,1)S(1)}, bf16[128,512]{1,0:T(8,128)(2,1)S(1)}, u32[]{:S(2)}, u32[]{:S(2)}) collective-permute-start(bf16[128,512]{1,0:T(8,128)(2,1)S(1)} %pad_maximum_fusion.1), channel_id=1, source_target_pairs={{0,2},{2,0},{4,6},{6,4},{8,10},{10,8},{12,14},{14,12},{1,3},{3,1},... | collective-permute-start | bytes 393224 | tf_op jit(solution)/shard_map/ppermute | solution.py:18
  38.5 1.4 %collective-permute-done.19 = bf16[128,512]{1,0:T(8,128)(2,1)S(1)} collective-permute-done((bf16[128,512]{1,0:T(8,128)(2,1)S(1)}, bf16[128,512]{1,0:T(8,128)(2,1)S(1)}, u32[]{:S(2)}, u32[]{:S(2)}) %collective-permute-start.19) | collective-permute-done | bytes 131104 | tf_op jit(solution)/shard_map/ppermute | solution.py:18
  41.9 0.6 collective-permute-done.4
  43.1 1.5 %collective-permute-done.20.other_ref = f32[512,128]{1,0:T(8,128)S(1)} collective-permute-done((f32[512,128]{1,0:T(8,128)S(1)}, f32[512,128]{1,0:T(8,128)S(1)}, u32[]{:S(2)}, u32[]{:S(2)}) %collective-permute-start.20) | collective-permute-done | bytes 262176 | tf_op jit(solution)/shard_map/ppermute | solution.py:18
  45.1 2.2 %collective-permute-start.24 = (f32[72,128]{1,0:T(8,128)S(1)}, f32[72,128]{1,0:T(8,128)S(1)}, u32[]{:S(2)}, u32[]{:S(2)}) collective-permute-start(f32[72,128]{1,0:T(8,128)S(1)} %make_gram.1), channel_id=1, source_target_pairs={{0,10},{1,15},{2,8},{3,13},{4,14},{5,11},{6,12},{7,9},{8,2},{9,7},... | collective-permute-start | bytes 110600 | tf_op jit(solution)/shard_map/ppermute | solution.py:36
  47.2 1.3 %collective-permute-start.23 = (f32[72,128]{1,0:T(8,128)S(1)}, f32[72,128]{1,0:T(8,128)S(1)}, u32[]{:S(2)}, u32[]{:S(2)}) collective-permute-start(f32[72,128]{1,0:T(8,128)S(1)} %make_gram.1), channel_id=1, source_target_pairs={{0,8},{1,13},{2,10},{3,15},{4,12},{5,9},{6,14},{7,11},{8,0},{9,5},... | collective-permute-start | bytes 110600 | tf_op jit(solution)/shard_map/ppermute | solution.py:36
  48.5 1.0 %collective-permute-start.22 = (f32[72,128]{1,0:T(8,128)S(1)}, f32[72,128]{1,0:T(8,128)S(1)}, u32[]{:S(2)}, u32[]{:S(2)}) collective-permute-start(f32[72,128]{1,0:T(8,128)S(1)} %make_gram.1), channel_id=1, source_target_pairs={{0,2},{1,7},{2,0},{3,5},{4,6},{5,3},{6,4},{7,1},{8,10},{9,15},{10,... | collective-permute-start | bytes 110600 | tf_op jit(solution)/shard_map/ppermute | solution.py:36
  49.5 0.7 collective-permute-start.21
  50.2 1.7 %collective-permute-done.24 = f32[72,128]{1,0:T(8,128)S(1)} collective-permute-done((f32[72,128]{1,0:T(8,128)S(1)}, f32[72,128]{1,0:T(8,128)S(1)}, u32[]{:S(2)}, u32[]{:S(2)}) %collective-permute-start.24) | collective-permute-done | bytes 36896 | tf_op jit(solution)/shard_map/ppermute | solution.py:36
  51.9 0.8 collective-permute-done.23
  52.7 1.5 %collective-permute-start.25 = (f32[72,128]{1,0:T(8,128)S(1)}, f32[72,128]{1,0:T(8,128)S(1)}, u32[]{:S(2)}, u32[]{:S(2)}) collective-permute-start(f32[72,128]{1,0:T(8,128)S(1)} %add_add_fusion), channel_id=1, source_target_pairs={{0,1},{1,0},{2,3},{3,2},{4,5},{5,4},{6,7},{7,6},{8,9},{9,8},{10,11... | collective-permute-start | bytes 110600 | tf_op jit(solution)/shard_map/ppermute | solution.py:18
  54.2 0.9 %collective-permute-done.25 = f32[72,128]{1,0:T(8,128)S(1)} collective-permute-done((f32[72,128]{1,0:T(8,128)S(1)}, f32[72,128]{1,0:T(8,128)S(1)}, u32[]{:S(2)}, u32[]{:S(2)}) %collective-permute-start.25) | collective-permute-done | bytes 36896 | tf_op jit(solution)/shard_map/ppermute | solution.py:18
  55.1 4.6 %make_basis.1 = (f32[512,128]{1,0:T(8,128)}, f32[128,2560]{1,0:T(8,128)S(1)}, f32[128,1536]{1,0:T(8,128)S(1)}) custom-call(f32[72,128]{1,0:T(8,128)S(1)} %add.128.gram_ref, f32[512,128]{1,0:T(8,128)S(1)} %fusion.2.mine_ref, f32[512,128]{1,0:T(8,128)S(1)} %collective-permute-done.20.other_ref, bf16[512,4096]{1,0:T(8,128)(2,1)} %slab_ref.3), custom_call_target="tpu_custom_call" | custom-call | tf_op jit(solution)/shard_map/make_basis/pallas_call | solution.py:321
  59.8 1.1 %collective-permute-start.26 = (bf16[4,1,16,2560]{3,2,1,0:T(8,128)(2,1)S(1)}, bf16[4,1,16,2560]{3,2,1,0:T(8,128)(2,1)S(1)}, u32[]{:S(2)}, u32[]{:S(2)}) collective-permute-start(bf16[4,1,16,2560]{3,2,1,0:T(8,128)(2,1)S(1)} %dynamic-slice_convert_fusion), channel_id=1, source_target_pairs={{0,2},{2,0},{4,6},{6,4},{8,10},{10,8},{12,14},{14,12},{1,3},{3,1},... | collective-permute-start | bytes 983048 | tf_op jit(solution)/shard_map/ppermute | solution.py:18
  60.9 1.8 %collective-permute-start.32 = (bf16[1,2,16,1536]{3,2,1,0:T(8,128)(2,1)S(1)}, bf16[1,2,16,1536]{3,2,1,0:T(8,128)(2,1)S(1)}, u32[]{:S(2)}, u32[]{:S(2)}) collective-permute-start(bf16[1,2,16,1536]{3,2,1,0:T(8,128)(2,1)S(1)} %get-tuple-element.30), channel_id=1, source_target_pairs={{0,12},{2,14},{4,8},{6,10},{8,4},{10,6},{12,0},{14,2},{1,13},{3,15... | collective-permute-start | bytes 294920 | tf_op jit(solution)/shard_map/ppermute | solution.py:18
  62.6 1.5 %collective-permute-start.31 = (bf16[1,2,16,1536]{3,2,1,0:T(8,128)(2,1)S(1)}, bf16[1,2,16,1536]{3,2,1,0:T(8,128)(2,1)S(1)}, u32[]{:S(2)}, u32[]{:S(2)}) collective-permute-start(bf16[1,2,16,1536]{3,2,1,0:T(8,128)(2,1)S(1)} %get-tuple-element.31), channel_id=1, source_target_pairs={{0,8},{2,10},{4,12},{6,14},{8,0},{10,2},{12,4},{14,6},{1,9},{3,11}... | collective-permute-start | bytes 294920 | tf_op jit(solution)/shard_map/ppermute | solution.py:18
  64.2 1.2 %collective-permute-start.30 = (bf16[1,2,16,1536]{3,2,1,0:T(8,128)(2,1)S(1)}, bf16[1,2,16,1536]{3,2,1,0:T(8,128)(2,1)S(1)}, u32[]{:S(2)}, u32[]{:S(2)}) collective-permute-start(bf16[1,2,16,1536]{3,2,1,0:T(8,128)(2,1)S(1)} %get-tuple-element.32), channel_id=1, source_target_pairs={{0,4},{2,6},{4,0},{6,2},{8,12},{10,14},{12,8},{14,10},{1,5},{3,7},... | collective-permute-start | bytes 294920 | tf_op jit(solution)/shard_map/ppermute | solution.py:18
  65.3 4.5 %collective-permute-done.26 = bf16[4,1,16,2560]{3,2,1,0:T(8,128)(2,1)S(1)} collective-permute-done((bf16[4,1,16,2560]{3,2,1,0:T(8,128)(2,1)S(1)}, bf16[4,1,16,2560]{3,2,1,0:T(8,128)(2,1)S(1)}, u32[]{:S(2)}, u32[]{:S(2)}) %collective-permute-start.26) | collective-permute-done | bytes 327712 | tf_op jit(solution)/shard_map/ppermute | solution.py:18
  69.9 3.3 %collective-permute-done.31 = bf16[1,2,16,1536]{3,2,1,0:T(8,128)(2,1)S(1)} collective-permute-done((bf16[1,2,16,1536]{3,2,1,0:T(8,128)(2,1)S(1)}, bf16[1,2,16,1536]{3,2,1,0:T(8,128)(2,1)S(1)}, u32[]{:S(2)}, u32[]{:S(2)}) %collective-permute-start.31) | collective-permute-done | bytes 98336 | tf_op jit(solution)/shard_map/ppermute | solution.py:18
  73.3 1.1 %collective-permute-start.33 = (bf16[1,1,16,1536]{3,2,1,0:T(8,128)(2,1)S(1)}, bf16[1,1,16,1536]{3,2,1,0:T(8,128)(2,1)S(1)}, u32[]{:S(2)}, u32[]{:S(2)}) collective-permute-start(bf16[1,1,16,1536]{3,2,1,0:T(8,128)(2,1)S(1)} %dynamic-slice_convert_fusion.7), channel_id=1, source_target_pairs={{0,2},{2,0},{4,6},{6,4},{8,10},{10,8},{12,14},{14,12},{1,3},{3,1},... | collective-permute-start | bytes 147464 | tf_op jit(solution)/shard_map/ppermute | solution.py:18
  74.4 1.9 %collective-permute-start.29 = (bf16[1,1,16,2560]{3,2,1,0:T(8,128)(2,1)S(1)}, bf16[1,1,16,2560]{3,2,1,0:T(8,128)(2,1)S(1)}, u32[]{:S(2)}, u32[]{:S(2)}) collective-permute-start(bf16[1,1,16,2560]{3,2,1,0:T(8,128)(2,1)S(1)} %get-tuple-element.33), channel_id=1, source_target_pairs={{0,12},{2,14},{4,8},{6,10},{8,4},{10,6},{12,0},{14,2},{1,13},{3,15... | collective-permute-start | bytes 245768 | tf_op jit(solution)/shard_map/ppermute | solution.py:18
  76.3 2.5 %collective-permute-start.27 = (bf16[1,1,16,2560]{3,2,1,0:T(8,128)(2,1)S(1)}, bf16[1,1,16,2560]{3,2,1,0:T(8,128)(2,1)S(1)}, u32[]{:S(2)}, u32[]{:S(2)}) collective-permute-start(bf16[1,1,16,2560]{3,2,1,0:T(8,128)(2,1)S(1)} %get-tuple-element.35), channel_id=1, source_target_pairs={{0,4},{2,6},{4,0},{6,2},{8,12},{10,14},{12,8},{14,10},{1,5},{3,7},... | collective-permute-start | bytes 245768 | tf_op jit(solution)/shard_map/ppermute | solution.py:18
  78.8 2.7 %collective-permute-done.29 = bf16[1,1,16,2560]{3,2,1,0:T(8,128)(2,1)S(1)} collective-permute-done((bf16[1,1,16,2560]{3,2,1,0:T(8,128)(2,1)S(1)}, bf16[1,1,16,2560]{3,2,1,0:T(8,128)(2,1)S(1)}, u32[]{:S(2)}, u32[]{:S(2)}) %collective-permute-start.29) | collective-permute-done | bytes 81952 | tf_op jit(solution)/shard_map/ppermute | solution.py:18
  81.5 1.7 %collective-permute-done.28 = bf16[1,1,16,2560]{3,2,1,0:T(8,128)(2,1)S(1)} collective-permute-done((bf16[1,1,16,2560]{3,2,1,0:T(8,128)(2,1)S(1)}, bf16[1,1,16,2560]{3,2,1,0:T(8,128)(2,1)S(1)}, u32[]{:S(2)}, u32[]{:S(2)}) %collective-permute-start.28) | collective-permute-done | bytes 81952 | tf_op jit(solution)/shard_map/ppermute | solution.py:18
  83.2 0.7 pad_maximum_fusion
  (74 shorter events, 4.9 us)
Async XLA Ops:
  0.6 0.9 %copy-start = (bf16[512,128]{1,0:T(8,128)(2,1)S(1)}, bf16[512,128]{1,0:T(8,128)(2,1)}, u32[]{:S(2)}) copy-start(bf16[512,128]{1,0:T(8,128)(2,1)} %start_ref.1) | copy-start | bytes 393220
  4.6 7.0 %collective-permute-start.15 = (bf16[128,512]{1,0:T(8,128)(2,1)S(1)}, bf16[128,512]{1,0:T(8,128)(2,1)S(1)}, u32[]{:S(2)}, u32[]{:S(2)}) collective-permute-start(bf16[128,512]{1,0:T(8,128)(2,1)S(1)} %select_convert_fusion), channel_id=1, source_target_pairs={{0,4},{2,6},{4,0},{6,2},{8,12},{10,14},{12,8},{14,10},{1,5},{3,7},... | collective-permute-start | bytes 393224 | tf_op jit(solution)/shard_map/ppermute | solution.py:18
  7.7 6.3 %collective-permute-start.10 = (bf16[128,512]{1,0:T(8,128)(2,1)S(1)}, bf16[128,512]{1,0:T(8,128)(2,1)S(1)}, u32[]{:S(2)}, u32[]{:S(2)}) collective-permute-start(bf16[128,512]{1,0:T(8,128)(2,1)S(1)} %select_convert_fusion.1), channel_id=1, source_target_pairs={{0,2},{2,0},{4,6},{6,4},{8,10},{10,8},{12,14},{14,12},{1,3},{3,1},... | collective-permute-start | bytes 393224 | tf_op jit(solution)/shard_map/ppermute | solution.py:18
  9.3 6.6 %collective-permute-start.5 = (bf16[128,512]{1,0:T(8,128)(2,1)S(1)}, bf16[128,512]{1,0:T(8,128)(2,1)S(1)}, u32[]{:S(2)}, u32[]{:S(2)}) collective-permute-start(bf16[128,512]{1,0:T(8,128)(2,1)S(1)} %select_convert_fusion.2), channel_id=1, source_target_pairs={{0,4},{2,6},{4,0},{6,2},{8,12},{10,14},{12,8},{14,10},{1,5},{3,7},... | collective-permute-start | bytes 393224 | tf_op jit(solution)/shard_map/ppermute | solution.py:18
  9.8 6.7 %collective-permute-start = (bf16[128,512]{1,0:T(8,128)(2,1)S(1)}, bf16[128,512]{1,0:T(8,128)(2,1)S(1)}, u32[]{:S(2)}, u32[]{:S(2)}) collective-permute-start(bf16[128,512]{1,0:T(8,128)(2,1)S(1)} %select_convert_fusion.3), channel_id=1, source_target_pairs={{0,2},{2,0},{4,6},{6,4},{8,10},{10,8},{12,14},{14,12},{1,3},{3,1},... | collective-permute-start | bytes 393224 | tf_op jit(solution)/shard_map/ppermute | solution.py:18
  11.7 6.5 %collective-permute-start.16 = (bf16[128,256]{1,0:T(8,128)(2,1)S(1)}, bf16[128,256]{1,0:T(8,128)(2,1)S(1)}, u32[]{:S(2)}, u32[]{:S(2)}) collective-permute-start(bf16[128,256]{1,0:T(8,128)(2,1)S(1)} %select_convert_fusion.4), channel_id=1, source_target_pairs={{0,2},{2,0},{4,6},{6,4},{8,10},{10,8},{12,14},{14,12},{1,3},{3,1},... | collective-permute-start | bytes 196616 | tf_op jit(solution)/shard_map/ppermute | solution.py:18
  14.1 25.9 %copy-start.1 = (bf16[512,4096]{1,0:T(8,128)(2,1)S(1)}, bf16[512,4096]{1,0:T(8,128)(2,1)}, u32[]{:S(2)}) copy-start(bf16[512,4096]{1,0:T(8,128)(2,1)} %slab_ref.3) | copy-start | bytes 12582916
  14.1 6.7 %collective-permute-start.11 = (bf16[128,256]{1,0:T(8,128)(2,1)S(1)}, bf16[128,256]{1,0:T(8,128)(2,1)S(1)}, u32[]{:S(2)}, u32[]{:S(2)}) collective-permute-start(bf16[128,256]{1,0:T(8,128)(2,1)S(1)} %select_convert_fusion.5), channel_id=1, source_target_pairs={{0,4},{2,6},{4,0},{6,2},{8,12},{10,14},{12,8},{14,10},{1,5},{3,7},... | collective-permute-start | bytes 196616 | tf_op jit(solution)/shard_map/ppermute | solution.py:18
  16.0 5.8 %collective-permute-start.6 = (bf16[128,256]{1,0:T(8,128)(2,1)S(1)}, bf16[128,256]{1,0:T(8,128)(2,1)S(1)}, u32[]{:S(2)}, u32[]{:S(2)}) collective-permute-start(bf16[128,256]{1,0:T(8,128)(2,1)S(1)} %select_convert_fusion.6), channel_id=1, source_target_pairs={{0,2},{2,0},{4,6},{6,4},{8,10},{10,8},{12,14},{14,12},{1,3},{3,1},... | collective-permute-start | bytes 196616 | tf_op jit(solution)/shard_map/ppermute | solution.py:18
  16.7 7.3 %collective-permute-start.1 = (bf16[128,256]{1,0:T(8,128)(2,1)S(1)}, bf16[128,256]{1,0:T(8,128)(2,1)S(1)}, u32[]{:S(2)}, u32[]{:S(2)}) collective-permute-start(bf16[128,256]{1,0:T(8,128)(2,1)S(1)} %select_convert_fusion.7), channel_id=1, source_target_pairs={{0,4},{2,6},{4,0},{6,2},{8,12},{10,14},{12,8},{14,10},{1,5},{3,7},... | collective-permute-start | bytes 196616 | tf_op jit(solution)/shard_map/ppermute | solution.py:18
  18.2 8.8 %collective-permute-start.17 = (bf16[128,256]{1,0:T(8,128)(2,1)S(1)}, bf16[128,256]{1,0:T(8,128)(2,1)S(1)}, u32[]{:S(2)}, u32[]{:S(2)}) collective-permute-start(bf16[128,256]{1,0:T(8,128)(2,1)S(1)} %fusion.25), channel_id=1, source_target_pairs={{0,8},{2,10},{4,12},{6,14},{8,0},{10,2},{12,4},{14,6},{1,9},{3,11}... | collective-permute-start | bytes 196616 | tf_op jit(solution)/shard_map/ppermute | solution.py:18
  20.9 9.1 %collective-permute-start.12 = (bf16[128,256]{1,0:T(8,128)(2,1)S(1)}, bf16[128,256]{1,0:T(8,128)(2,1)S(1)}, u32[]{:S(2)}, u32[]{:S(2)}) collective-permute-start(bf16[128,256]{1,0:T(8,128)(2,1)S(1)} %fusion.24), channel_id=1, source_target_pairs={{0,8},{2,10},{4,12},{6,14},{8,0},{10,2},{12,4},{14,6},{1,9},{3,11}... | collective-permute-start | bytes 196616 | tf_op jit(solution)/shard_map/ppermute | solution.py:18
  21.8 9.3 %collective-permute-start.7 = (bf16[128,256]{1,0:T(8,128)(2,1)S(1)}, bf16[128,256]{1,0:T(8,128)(2,1)S(1)}, u32[]{:S(2)}, u32[]{:S(2)}) collective-permute-start(bf16[128,256]{1,0:T(8,128)(2,1)S(1)} %fusion.23), channel_id=1, source_target_pairs={{0,8},{2,10},{4,12},{6,14},{8,0},{10,2},{12,4},{14,6},{1,9},{3,11}... | collective-permute-start | bytes 196616 | tf_op jit(solution)/shard_map/ppermute | solution.py:18
  24.0 8.3 %collective-permute-start.2 = (bf16[128,256]{1,0:T(8,128)(2,1)S(1)}, bf16[128,256]{1,0:T(8,128)(2,1)S(1)}, u32[]{:S(2)}, u32[]{:S(2)}) collective-permute-start(bf16[128,256]{1,0:T(8,128)(2,1)S(1)} %fusion.22), channel_id=1, source_target_pairs={{0,8},{2,10},{4,12},{6,14},{8,0},{10,2},{12,4},{14,6},{1,9},{3,11}... | collective-permute-start | bytes 196616 | tf_op jit(solution)/shard_map/ppermute | solution.py:18
  27.1 6.4 %collective-permute-start.18 = (bf16[128,256]{1,0:T(8,128)(2,1)S(1)}, bf16[128,256]{1,0:T(8,128)(2,1)S(1)}, u32[]{:S(2)}, u32[]{:S(2)}) collective-permute-start(bf16[128,256]{1,0:T(8,128)(2,1)S(1)} %multiply_convert_fusion), channel_id=1, source_target_pairs={{0,2},{2,0},{4,6},{6,4},{8,10},{10,8},{12,14},{14,12},{1,3},{3,1},... | collective-permute-start | bytes 196616 | tf_op jit(solution)/shard_map/ppermute | solution.py:18
  30.0 5.0 %collective-permute-start.13 = (bf16[128,256]{1,0:T(8,128)(2,1)S(1)}, bf16[128,256]{1,0:T(8,128)(2,1)S(1)}, u32[]{:S(2)}, u32[]{:S(2)}) collective-permute-start(bf16[128,256]{1,0:T(8,128)(2,1)S(1)} %multiply_convert_fusion.1), channel_id=1, source_target_pairs={{0,4},{2,6},{4,0},{6,2},{8,12},{10,14},{12,8},{14,10},{1,5},{3,7},... | collective-permute-start | bytes 196616 | tf_op jit(solution)/shard_map/ppermute | solution.py:18
  31.1 5.2 %collective-permute-start.8 = (bf16[128,256]{1,0:T(8,128)(2,1)S(1)}, bf16[128,256]{1,0:T(8,128)(2,1)S(1)}, u32[]{:S(2)}, u32[]{:S(2)}) collective-permute-start(bf16[128,256]{1,0:T(8,128)(2,1)S(1)} %multiply_convert_fusion.2), channel_id=1, source_target_pairs={{0,2},{2,0},{4,6},{6,4},{8,10},{10,8},{12,14},{14,12},{1,3},{3,1},... | collective-permute-start | bytes 196616 | tf_op jit(solution)/shard_map/ppermute | solution.py:18
  32.3 5.1 %collective-permute-start.3 = (bf16[128,256]{1,0:T(8,128)(2,1)S(1)}, bf16[128,256]{1,0:T(8,128)(2,1)S(1)}, u32[]{:S(2)}, u32[]{:S(2)}) collective-permute-start(bf16[128,256]{1,0:T(8,128)(2,1)S(1)} %multiply_convert_fusion.3), channel_id=1, source_target_pairs={{0,4},{2,6},{4,0},{6,2},{8,12},{10,14},{12,8},{14,10},{1,5},{3,7},... | collective-permute-start | bytes 196616 | tf_op jit(solution)/shard_map/ppermute | solution.py:18
  33.5 6.4 %collective-permute-start.19 = (bf16[128,512]{1,0:T(8,128)(2,1)S(1)}, bf16[128,512]{1,0:T(8,128)(2,1)S(1)}, u32[]{:S(2)}, u32[]{:S(2)}) collective-permute-start(bf16[128,512]{1,0:T(8,128)(2,1)S(1)} %pad_maximum_fusion.4), channel_id=1, source_target_pairs={{0,4},{2,6},{4,0},{6,2},{8,12},{10,14},{12,8},{14,10},{1,5},{3,7},... | collective-permute-start | bytes 393224 | tf_op jit(solution)/shard_map/ppermute | solution.py:18
  35.1 5.6 %collective-permute-start.14 = (bf16[128,512]{1,0:T(8,128)(2,1)S(1)}, bf16[128,512]{1,0:T(8,128)(2,1)S(1)}, u32[]{:S(2)}, u32[]{:S(2)}) collective-permute-start(bf16[128,512]{1,0:T(8,128)(2,1)S(1)} %pad_maximum_fusion.3), channel_id=1, source_target_pairs={{0,2},{2,0},{4,6},{6,4},{8,10},{10,8},{12,14},{14,12},{1,3},{3,1},... | collective-permute-start | bytes 393224 | tf_op jit(solution)/shard_map/ppermute | solution.py:18
  36.3 5.0 %collective-permute-start.9 = (bf16[128,512]{1,0:T(8,128)(2,1)S(1)}, bf16[128,512]{1,0:T(8,128)(2,1)S(1)}, u32[]{:S(2)}, u32[]{:S(2)}) collective-permute-start(bf16[128,512]{1,0:T(8,128)(2,1)S(1)} %pad_maximum_fusion.2), channel_id=1, source_target_pairs={{0,4},{2,6},{4,0},{6,2},{8,12},{10,14},{12,8},{14,10},{1,5},{3,7},... | collective-permute-start | bytes 393224 | tf_op jit(solution)/shard_map/ppermute | solution.py:18
  37.5 5.0 %collective-permute-start.4 = (bf16[128,512]{1,0:T(8,128)(2,1)S(1)}, bf16[128,512]{1,0:T(8,128)(2,1)S(1)}, u32[]{:S(2)}, u32[]{:S(2)}) collective-permute-start(bf16[128,512]{1,0:T(8,128)(2,1)S(1)} %pad_maximum_fusion.1), channel_id=1, source_target_pairs={{0,2},{2,0},{4,6},{6,4},{8,10},{10,8},{12,14},{14,12},{1,3},{3,1},... | collective-permute-start | bytes 393224 | tf_op jit(solution)/shard_map/ppermute | solution.py:18
  43.0 1.6 %collective-permute-start.20 = (f32[512,128]{1,0:T(8,128)S(1)}, f32[512,128]{1,0:T(8,128)S(1)}, u32[]{:S(2)}, u32[]{:S(2)}) collective-permute-start(f32[512,128]{1,0:T(8,128)S(1)} %fusion.2.mine_ref), channel_id=1, source_target_pairs={{0,1},{1,0},{2,3},{3,2},{4,5},{5,4},{6,7},{7,6},{8,9},{9,8},{10,11... | collective-permute-start | bytes 786440 | tf_op jit(solution)/shard_map/ppermute | solution.py:18
  45.1 6.8 %collective-permute-start.24 = (f32[72,128]{1,0:T(8,128)S(1)}, f32[72,128]{1,0:T(8,128)S(1)}, u32[]{:S(2)}, u32[]{:S(2)}) collective-permute-start(f32[72,128]{1,0:T(8,128)S(1)} %make_gram.1), channel_id=1, source_target_pairs={{0,10},{1,15},{2,8},{3,13},{4,14},{5,11},{6,12},{7,9},{8,2},{9,7},... | collective-permute-start | bytes 110600 | tf_op jit(solution)/shard_map/ppermute | solution.py:36
  47.2 5.5 %collective-permute-start.23 = (f32[72,128]{1,0:T(8,128)S(1)}, f32[72,128]{1,0:T(8,128)S(1)}, u32[]{:S(2)}, u32[]{:S(2)}) collective-permute-start(f32[72,128]{1,0:T(8,128)S(1)} %make_gram.1), channel_id=1, source_target_pairs={{0,8},{1,13},{2,10},{3,15},{4,12},{5,9},{6,14},{7,11},{8,0},{9,5},... | collective-permute-start | bytes 110600 | tf_op jit(solution)/shard_map/ppermute | solution.py:36
  48.5 4.2 %collective-permute-start.22 = (f32[72,128]{1,0:T(8,128)S(1)}, f32[72,128]{1,0:T(8,128)S(1)}, u32[]{:S(2)}, u32[]{:S(2)}) collective-permute-start(f32[72,128]{1,0:T(8,128)S(1)} %make_gram.1), channel_id=1, source_target_pairs={{0,2},{1,7},{2,0},{3,5},{4,6},{5,3},{6,4},{7,1},{8,10},{9,15},{10,... | collective-permute-start | bytes 110600 | tf_op jit(solution)/shard_map/ppermute | solution.py:36
  49.5 3.2 %collective-permute-start.21 = (f32[72,128]{1,0:T(8,128)S(1)}, f32[72,128]{1,0:T(8,128)S(1)}, u32[]{:S(2)}, u32[]{:S(2)}) collective-permute-start(f32[72,128]{1,0:T(8,128)S(1)} %make_gram.1), channel_id=1, source_target_pairs={{1,5},{3,7},{5,1},{7,3},{9,13},{11,15},{13,9},{15,11},{17,21},{19,... | collective-permute-start | bytes 110600 | tf_op jit(solution)/shard_map/ppermute | solution.py:36
  52.7 2.4 %collective-permute-start.25 = (f32[72,128]{1,0:T(8,128)S(1)}, f32[72,128]{1,0:T(8,128)S(1)}, u32[]{:S(2)}, u32[]{:S(2)}) collective-permute-start(f32[72,128]{1,0:T(8,128)S(1)} %add_add_fusion), channel_id=1, source_target_pairs={{0,1},{1,0},{2,3},{3,2},{4,5},{5,4},{6,7},{7,6},{8,9},{9,8},{10,11... | collective-permute-start | bytes 110600 | tf_op jit(solution)/shard_map/ppermute | solution.py:18
  59.8 10.0 %collective-permute-start.26 = (bf16[4,1,16,2560]{3,2,1,0:T(8,128)(2,1)S(1)}, bf16[4,1,16,2560]{3,2,1,0:T(8,128)(2,1)S(1)}, u32[]{:S(2)}, u32[]{:S(2)}) collective-permute-start(bf16[4,1,16,2560]{3,2,1,0:T(8,128)(2,1)S(1)} %dynamic-slice_convert_fusion), channel_id=1, source_target_pairs={{0,2},{2,0},{4,6},{6,4},{8,10},{10,8},{12,14},{14,12},{1,3},{3,1},... | collective-permute-start | bytes 983048 | tf_op jit(solution)/shard_map/ppermute | solution.py:18
  60.9 9.1 %collective-permute-start.32 = (bf16[1,2,16,1536]{3,2,1,0:T(8,128)(2,1)S(1)}, bf16[1,2,16,1536]{3,2,1,0:T(8,128)(2,1)S(1)}, u32[]{:S(2)}, u32[]{:S(2)}) collective-permute-start(bf16[1,2,16,1536]{3,2,1,0:T(8,128)(2,1)S(1)} %get-tuple-element.30), channel_id=1, source_target_pairs={{0,12},{2,14},{4,8},{6,10},{8,4},{10,6},{12,0},{14,2},{1,13},{3,15... | collective-permute-start | bytes 294920 | tf_op jit(solution)/shard_map/ppermute | solution.py:18
  62.6 10.6 %collective-permute-start.31 = (bf16[1,2,16,1536]{3,2,1,0:T(8,128)(2,1)S(1)}, bf16[1,2,16,1536]{3,2,1,0:T(8,128)(2,1)S(1)}, u32[]{:S(2)}, u32[]{:S(2)}) collective-permute-start(bf16[1,2,16,1536]{3,2,1,0:T(8,128)(2,1)S(1)} %get-tuple-element.31), channel_id=1, source_target_pairs={{0,8},{2,10},{4,12},{6,14},{8,0},{10,2},{12,4},{14,6},{1,9},{3,11}... | collective-permute-start | bytes 294920 | tf_op jit(solution)/shard_map/ppermute | solution.py:18
  64.2 9.1 %collective-permute-start.30 = (bf16[1,2,16,1536]{3,2,1,0:T(8,128)(2,1)S(1)}, bf16[1,2,16,1536]{3,2,1,0:T(8,128)(2,1)S(1)}, u32[]{:S(2)}, u32[]{:S(2)}) collective-permute-start(bf16[1,2,16,1536]{3,2,1,0:T(8,128)(2,1)S(1)} %get-tuple-element.32), channel_id=1, source_target_pairs={{0,4},{2,6},{4,0},{6,2},{8,12},{10,14},{12,8},{14,10},{1,5},{3,7},... | collective-permute-start | bytes 294920 | tf_op jit(solution)/shard_map/ppermute | solution.py:18
  73.3 5.5 %collective-permute-start.33 = (bf16[1,1,16,1536]{3,2,1,0:T(8,128)(2,1)S(1)}, bf16[1,1,16,1536]{3,2,1,0:T(8,128)(2,1)S(1)}, u32[]{:S(2)}, u32[]{:S(2)}) collective-permute-start(bf16[1,1,16,1536]{3,2,1,0:T(8,128)(2,1)S(1)} %dynamic-slice_convert_fusion.7), channel_id=1, source_target_pairs={{0,2},{2,0},{4,6},{6,4},{8,10},{10,8},{12,14},{14,12},{1,3},{3,1},... | collective-permute-start | bytes 147464 | tf_op jit(solution)/shard_map/ppermute | solution.py:18
  74.4 7.1 %collective-permute-start.29 = (bf16[1,1,16,2560]{3,2,1,0:T(8,128)(2,1)S(1)}, bf16[1,1,16,2560]{3,2,1,0:T(8,128)(2,1)S(1)}, u32[]{:S(2)}, u32[]{:S(2)}) collective-permute-start(bf16[1,1,16,2560]{3,2,1,0:T(8,128)(2,1)S(1)} %get-tuple-element.33), channel_id=1, source_target_pairs={{0,12},{2,14},{4,8},{6,10},{8,4},{10,6},{12,0},{14,2},{1,13},{3,15... | collective-permute-start | bytes 245768 | tf_op jit(solution)/shard_map/ppermute | solution.py:18
  76.3 6.9 %collective-permute-start.28 = (bf16[1,1,16,2560]{3,2,1,0:T(8,128)(2,1)S(1)}, bf16[1,1,16,2560]{3,2,1,0:T(8,128)(2,1)S(1)}, u32[]{:S(2)}, u32[]{:S(2)}) collective-permute-start(bf16[1,1,16,2560]{3,2,1,0:T(8,128)(2,1)S(1)} %get-tuple-element.34), channel_id=1, source_target_pairs={{0,8},{2,10},{4,12},{6,14},{8,0},{10,2},{12,4},{14,6},{1,9},{3,11}... | collective-permute-start | bytes 245768 | tf_op jit(solution)/shard_map/ppermute | solution.py:18
  76.3 6.9 %collective-permute-start.27 = (bf16[1,1,16,2560]{3,2,1,0:T(8,128)(2,1)S(1)}, bf16[1,1,16,2560]{3,2,1,0:T(8,128)(2,1)S(1)}, u32[]{:S(2)}, u32[]{:S(2)}) collective-permute-start(bf16[1,1,16,2560]{3,2,1,0:T(8,128)(2,1)S(1)} %get-tuple-element.35), channel_id=1, source_target_pairs={{0,4},{2,6},{4,0},{6,2},{8,12},{10,14},{12,8},{14,10},{1,5},{3,7},... | collective-permute-start | bytes 245768 | tf_op jit(solution)/shard_map/ppermute | solution.py:18

commit v17 on v15

--- a/solution.py
+++ b/solution.py
@@ -42,50 +42,67 @@
     return value
 
 
-def scatter_sum(value, axis, order):
-    rows, cols = value.shape[0] >> len(order), value.shape[1]
-    total = value.reshape([2] * len(order) + [rows, cols])
-    left = sorted(order, reverse=True)
-    for bit in order:
-        dim = left.index(bit)
-        left.remove(bit)
-        low = lax.index_in_dim(total, 0, dim, keepdims=False)
-        high = lax.index_in_dim(total, 1, dim, keepdims=False)
-        upper = bit_of(axis, bit) == 1
-        send = jnp.where(upper, low, high).astype(jnp.bfloat16)
-        landed = swap(send, axis, 1 << bit)
-        total = jnp.where(upper, high, low) + landed.astype(jnp.float32)
-    return total
-
-
 def bit_of(axis, bit):
     return lax.rem(lax.div(lax.axis_index(axis), 1 << bit), 2)
 
 
-def sum_and_share(value, axis, order, scale):
-    for bit in order[:-1]:
-        upper = bit_of(axis, bit) == 1
-        half = value.shape[1] // 2
-        low, high = value[:, :half], value[:, half:]
-        send = jnp.where(upper, low, high).astype(jnp.bfloat16)
-        landed = swap(send, axis, 1 << bit)
-        value = jnp.where(upper, high, low) + landed.astype(jnp.float32)
-    landed = swap(value.astype(jnp.bfloat16), axis, 1 << order[-1])
-    block = ((value + landed.astype(jnp.float32)) * scale).astype(jnp.bfloat16)
-    for bit in reversed(order[:-1]):
-        upper = bit_of(axis, bit) == 1
-        other = swap(block, axis, 1 << bit)
-        block = jnp.concatenate(
-            [jnp.where(upper, other, block), jnp.where(upper, block, other)], axis=1
-        )
-    return block
-
-
-def orders_of(axis):
-    bits = list(range((lax.axis_size(axis) - 1).bit_length()))
-    if len(bits) < 3:
-        return [bits, bits]
-    return [bits, [bits[1], bits[0]] + bits[2:]]
+def halve_columns(value, axis, bit):
+    upper = bit_of(axis, bit) == 1
+    half = value.shape[1] // 2
+    low, high = value[:, :half], value[:, half:]
+    landed = swap(jnp.where(upper, low, high).astype(jnp.bfloat16), axis, 1 << bit)
+    return jnp.where(upper, high, low) + landed.astype(jnp.float32)
+
+
+def join_columns(block, axis, bit):
+    upper = bit_of(axis, bit) == 1
+    other = swap(block, axis, 1 << bit)
+    return jnp.concatenate(
+        [jnp.where(upper, other, block), jnp.where(upper, block, other)], axis=1
+    )
+
+
+def sum_and_share(first, second, axis, scale):
+    bits = (lax.axis_size(axis) - 1).bit_length()
+    first = halve_columns(first, axis, 0)
+    second = halve_columns(second, axis, 1)
+    first = halve_columns(first, axis, 1)
+    second = halve_columns(second, axis, 0)
+    both = jnp.concatenate([first, second], axis=1)
+    for bit in range(2, bits - 1):
+        both = halve_columns(both, axis, bit)
+    landed = swap(both.astype(jnp.bfloat16), axis, 1 << (bits - 1))
+    block = ((both + landed.astype(jnp.float32)) * scale).astype(jnp.bfloat16)
+    for bit in reversed(range(2, bits - 1)):
+        block = join_columns(block, axis, bit)
+    half = block.shape[1] // 2
+    first, second = block[:, :half], block[:, half:]
+    first = join_columns(first, axis, 1)
+    second = join_columns(second, axis, 0)
+    return join_columns(first, axis, 0), join_columns(second, axis, 1)
+
+
+def halve_rows(value, axis, bit, dim):
+    upper = bit_of(axis, bit) == 1
+    low = lax.index_in_dim(value, 0, dim, keepdims=False)
+    high = lax.index_in_dim(value, 1, dim, keepdims=False)
+    landed = swap(jnp.where(upper, low, high).astype(jnp.bfloat16), axis, 1 << bit)
+    return jnp.where(upper, high, low) + landed.astype(jnp.float32)
+
+
+def scatter_sum(first, second, axis):
+    n = lax.axis_size(axis)
+    rows, cols = first.shape[0] // n, first.shape[1]
+    shape = (n // 4, 2, 2, rows, cols)
+    first = halve_rows(first.reshape(shape), axis, 0, 2)
+    second = halve_rows(second.reshape(shape), axis, 1, 1)
+    first = halve_rows(first, axis, 1, 1)
+    second = halve_rows(second, axis, 0, 1)
+    both = jnp.concatenate([first, second], axis=-1)
+    for bit in range(2, (n - 1).bit_length()):
+        both = both.reshape(both.shape[0] // 2, 2, rows, 2 * cols)
+        both = halve_rows(both, axis, bit, 1)
+    return both.reshape(rows, 2 * cols)
 
 
 def fetch_tiles(slab_ref, buffer, arrived):
@@ -303,17 +320,16 @@
 
     local_cols = first_product(start_sketch, activations, CHUNKS)
     partial_sketch = 0.0
-    orders = orders_of("row")
     step = cols_here // CHUNKS
-    for c in range(CHUNKS):
-        span = slice(c * step, (c + 1) * step)
-        shared = sum_and_share(local_cols[c], "row", orders[c % 2], 1.0 / root_rows)
-        partial_sketch = partial_sketch + lax.dot_general(
-            activations[:, span],
-            shared,
-            (((1,), (1,)), ((), ())),
-            preferred_element_type=jnp.float32,
-        )
+    for c in range(0, CHUNKS, 2):
+        shared = sum_and_share(local_cols[c], local_cols[c + 1], "row", 1.0 / root_rows)
+        for i in range(2):
+            partial_sketch = partial_sketch + lax.dot_general(
+                activations[:, (c + i) * step : (c + i + 1) * step],
+                shared[i],
+                (((1,), (1,)), ((), ())),
+                preferred_element_type=jnp.float32,
+            )
     other_sketch = swap(partial_sketch, "col", 1)
     gram = row_sum(make_gram(partial_sketch, other_sketch, total_cols))
     basis, *products = make_basis(
@@ -321,8 +337,8 @@
     )
 
     pieces = [
-        scatter_sum(product, "row", orders[c % 2]) / total_rows
-        for c, product in enumerate(products)
+        scatter_sum(products[c], products[c + 1], "row") / total_rows
+        for c in range(0, CHUNKS, 2)
     ]
     return (basis, jnp.concatenate(pieces, axis=1))
 

time: 82.8 us -> 83.9 us (1.013)
  waiting for transfers between devices: 19.5 us -> 24.5 us
  starting transfers between devices: 49 us -> 45.1 us
    ppermute x34 -> x30, starting transfers between devices: 43.9 us -> 40 us  [swap(): return lax.ppermute(value, axis, [(i, i ^ distance) for i in range(size)])]
    ppermute x34 -> x30, waiting for transfers between devices: 17 us -> 20.9 us  [swap(): return lax.ppermute(value, axis, [(i, i ^ distance) for i in range(size)])]
    ppermute x4, waiting for transfers between devices: 2.47 us -> 3.61 us  [row_sum(): terms.append(lax.ppermute(value, ('row', 'col'), pairs))]
  transfers between devices with their start and end apart: 38 -> 34, of which waited for: 18 -> 16; matrix products, arithmetic and copies ran while one was open for 3% -> 3% of each run, Pallas kernels for 0% -> 0%
where the time goes in v17:
time: 83.9 us; the launch traced here: 83.8 us
  starting transfers between devices  45.1 us (54%)
  waiting for transfers between devices  24.5 us (29%)
  Pallas kernels  8.12 us (10%)
  other arithmetic  2.13 us (3%)
  matrix products  1.74 us (2%)
  between operations  1.12 us (1%)
  local copies, waits for them, and re-layouts  1.07 us (1%)
    ppermute x30, starting transfers between devices, swap(): return lax.ppermute(value, axis, [(i, i ^ distance) for i in range(size)])  40 us
    ppermute x30, waiting for transfers between devices, swap(): return lax.ppermute(value, axis, [(i, i ^ distance) for i in range(size)])  20.9 us
    ppermute x4, starting transfers between devices, row_sum(): terms.append(lax.ppermute(value, ('row', 'col'), pairs))  5.1 us
    pallas_call x1, Pallas kernels, make_basis(): pl.pallas_call(functools.partial(basis_kernel, total_cols, root_rows), ou...  4.63 us
    ppermute x4, waiting for transfers between devices, row_sum(): terms.append(lax.ppermute(value, ('row', 'col'), pairs))  3.61 us
    pallas_call x1, Pallas kernels, first_product(): pl.pallas_call(sketch_kernel, out_shape=[jax.ShapeDtypeStruct((width, col...  2.99 us
    dot_general x4, matrix products, per_device(): lax.dot_general(activations[:, (c + i) * step:(c + i + 1) * step], shared...  1.74 us
  transfers between devices with their start and end apart: 34, of which 16 were waited for; matrix products, arithmetic and copies ran while one was open for 3% of the time, Pallas kernels for 0%

profile of v17, /device:TPU:0, one launch (start us, length us, event | category | flops | bytes accessed | tf_op | source)
XLA Modules:
  0.0 83.8 jit_solution(14213750379954827091)
XLA Ops:
  0.7 0.9 %copy-done = bf16[512,128]{1,0:T(8,128)(2,1)S(1)} copy-done((bf16[512,128]{1,0:T(8,128)(2,1)S(1)}, bf16[512,128]{1,0:T(8,128)(2,1)}, u32[]{:S(2)}) %copy-start) | copy-done | bytes 131096
  1.6 3.0 %first_product.1 = (f32[128,1024]{1,0:T(8,128)S(1)}, f32[128,1024]{1,0:T(8,128)S(1)}, f32[128,1024]{1,0:T(8,128)S(1)}, f32[128,1024]{1,0:T(8,128)S(1)}) custom-call(bf16[512,128]{1,0:T(8,128)(2,1)S(1)} %copy-done, bf16[512,4096]{1,0:T(8,128)(2,1)} %slab_ref.3), custom_call_target="tpu_custom_call" | custom-call | flops 536870912 | bytes 4194304 | tf_op jit(solution)/shard_map/first_product/pallas_call | solution.py:135
  4.6 3.1 %collective-permute-start.11 = (bf16[128,512]{1,0:T(8,128)(2,1)S(1)}, bf16[128,512]{1,0:T(8,128)(2,1)S(1)}, u32[]{:S(2)}, u32[]{:S(2)}) collective-permute-start(bf16[128,512]{1,0:T(8,128)(2,1)S(1)} %select_convert_fusion.4), channel_id=1, source_target_pairs={{0,4},{2,6},{4,0},{6,2},{8,12},{10,14},{12,8},{14,10},{1,5},{3,7},... | collective-permute-start | bytes 393224 | tf_op jit(solution)/shard_map/ppermute | solution.py:18
  7.7 1.6 %collective-permute-start.9 = (bf16[128,512]{1,0:T(8,128)(2,1)S(1)}, bf16[128,512]{1,0:T(8,128)(2,1)S(1)}, u32[]{:S(2)}, u32[]{:S(2)}) collective-permute-start(bf16[128,512]{1,0:T(8,128)(2,1)S(1)} %select_convert_fusion.5), channel_id=1, source_target_pairs={{0,2},{2,0},{4,6},{6,4},{8,10},{10,8},{12,14},{14,12},{1,3},{3,1},... | collective-permute-start | bytes 393224 | tf_op jit(solution)/shard_map/ppermute | solution.py:18
  9.3 0.5 collective-permute-start.2
  10.0 1.6 %collective-permute-done.11 = bf16[128,512]{1,0:T(8,128)(2,1)S(1)} collective-permute-done((bf16[128,512]{1,0:T(8,128)(2,1)S(1)}, bf16[128,512]{1,0:T(8,128)(2,1)S(1)}, u32[]{:S(2)}, u32[]{:S(2)}) %collective-permute-start.11) | collective-permute-done | bytes 131104 | tf_op jit(solution)/shard_map/ppermute | solution.py:18
  11.7 2.4 %collective-permute-start.12 = (bf16[128,256]{1,0:T(8,128)(2,1)S(1)}, bf16[128,256]{1,0:T(8,128)(2,1)S(1)}, u32[]{:S(2)}, u32[]{:S(2)}) collective-permute-start(bf16[128,256]{1,0:T(8,128)(2,1)S(1)} %select_convert_fusion.14), channel_id=1, source_target_pairs={{0,2},{2,0},{4,6},{6,4},{8,10},{10,8},{12,14},{14,12},{1,3},{3,1},... | collective-permute-start | bytes 196616 | tf_op jit(solution)/shard_map/ppermute | solution.py:18
  14.1 1.7 %collective-permute-start.10 = (bf16[128,256]{1,0:T(8,128)(2,1)S(1)}, bf16[128,256]{1,0:T(8,128)(2,1)S(1)}, u32[]{:S(2)}, u32[]{:S(2)}) collective-permute-start(bf16[128,256]{1,0:T(8,128)(2,1)S(1)} %select_convert_fusion.15), channel_id=1, source_target_pairs={{0,4},{2,6},{4,0},{6,2},{8,12},{10,14},{12,8},{14,10},{1,5},{3,7},... | collective-permute-start | bytes 196616 | tf_op jit(solution)/shard_map/ppermute | solution.py:18
  16.0 0.6 collective-permute-start.3
  16.7 1.5 %collective-permute-start.1 = (bf16[128,256]{1,0:T(8,128)(2,1)S(1)}, bf16[128,256]{1,0:T(8,128)(2,1)S(1)}, u32[]{:S(2)}, u32[]{:S(2)}) collective-permute-start(bf16[128,256]{1,0:T(8,128)(2,1)S(1)} %select_convert_fusion.17), channel_id=1, source_target_pairs={{0,4},{2,6},{4,0},{6,2},{8,12},{10,14},{12,8},{14,10},{1,5},{3,7},... | collective-permute-start | bytes 196616 | tf_op jit(solution)/shard_map/ppermute | solution.py:18
  18.2 0.5 collective-permute-done.10
  18.8 3.0 %collective-permute-start.13 = (bf16[128,512]{1,0:T(8,128)(2,1)S(1)}, bf16[128,512]{1,0:T(8,128)(2,1)S(1)}, u32[]{:S(2)}, u32[]{:S(2)}) collective-permute-start(bf16[128,512]{1,0:T(8,128)(2,1)S(1)} %fusion.22), channel_id=1, source_target_pairs={{0,8},{2,10},{4,12},{6,14},{8,0},{10,2},{12,4},{14,6},{1,9},{3,11}... | collective-permute-start | bytes 393224 | tf_op jit(solution)/shard_map/ppermute | solution.py:18
  21.9 2.1 %collective-permute-start.4 = (bf16[128,512]{1,0:T(8,128)(2,1)S(1)}, bf16[128,512]{1,0:T(8,128)(2,1)S(1)}, u32[]{:S(2)}, u32[]{:S(2)}) collective-permute-start(bf16[128,512]{1,0:T(8,128)(2,1)S(1)} %fusion.23), channel_id=1, source_target_pairs={{0,8},{2,10},{4,12},{6,14},{8,0},{10,2},{12,4},{14,6},{1,9},{3,11}... | collective-permute-start | bytes 393224 | tf_op jit(solution)/shard_map/ppermute | solution.py:18
  24.0 5.4 %collective-permute-done.13 = bf16[128,512]{1,0:T(8,128)(2,1)S(1)} collective-permute-done((bf16[128,512]{1,0:T(8,128)(2,1)S(1)}, bf16[128,512]{1,0:T(8,128)(2,1)S(1)}, u32[]{:S(2)}, u32[]{:S(2)}) %collective-permute-start.13) | collective-permute-done | bytes 131104 | tf_op jit(solution)/shard_map/ppermute | solution.py:18
  29.7 1.0 %collective-permute-start.16 = (bf16[128,256]{1,0:T(8,128)(2,1)S(1)}, bf16[128,256]{1,0:T(8,128)(2,1)S(1)}, u32[]{:S(2)}, u32[]{:S(2)}) collective-permute-start(bf16[128,256]{1,0:T(8,128)(2,1)S(1)} %get-tuple-element.51), channel_id=1, source_target_pairs={{0,2},{2,0},{4,6},{6,4},{8,10},{10,8},{12,14},{14,12},{1,3},{3,1},... | collective-permute-start | bytes 196616 | tf_op jit(solution)/shard_map/ppermute | solution.py:18
  30.9 2.0 %collective-permute-start.5 = (bf16[128,256]{1,0:T(8,128)(2,1)S(1)}, bf16[128,256]{1,0:T(8,128)(2,1)S(1)}, u32[]{:S(2)}, u32[]{:S(2)}) collective-permute-start(bf16[128,256]{1,0:T(8,128)(2,1)S(1)} %get-tuple-element.46), channel_id=1, source_target_pairs={{0,4},{2,6},{4,0},{6,2},{8,12},{10,14},{12,8},{14,10},{1,5},{3,7},... | collective-permute-start | bytes 196616 | tf_op jit(solution)/shard_map/ppermute | solution.py:18
  32.8 0.9 %collective-permute-start.7 = (bf16[128,256]{1,0:T(8,128)(2,1)S(1)}, bf16[128,256]{1,0:T(8,128)(2,1)S(1)}, u32[]{:S(2)}, u32[]{:S(2)}) collective-permute-start(bf16[128,256]{1,0:T(8,128)(2,1)S(1)} %get-tuple-element.47), channel_id=1, source_target_pairs={{0,2},{2,0},{4,6},{6,4},{8,10},{10,8},{12,14},{14,12},{1,3},{3,1},... | collective-permute-start | bytes 196616 | tf_op jit(solution)/shard_map/ppermute | solution.py:18
  33.7 0.7 collective-permute-done.14
  34.5 2.2 %collective-permute-start.17 = (bf16[128,512]{1,0:T(8,128)(2,1)S(1)}, bf16[128,512]{1,0:T(8,128)(2,1)S(1)}, u32[]{:S(2)}, u32[]{:S(2)}) collective-permute-start(bf16[128,512]{1,0:T(8,128)(2,1)S(1)} %pad_maximum_fusion.6), channel_id=1, source_target_pairs={{0,4},{2,6},{4,0},{6,2},{8,12},{10,14},{12,8},{14,10},{1,5},{3,7},... | collective-permute-start | bytes 393224 | tf_op jit(solution)/shard_map/ppermute | solution.py:18
  36.7 1.2 %collective-permute-start.15 = (bf16[128,512]{1,0:T(8,128)(2,1)S(1)}, bf16[128,512]{1,0:T(8,128)(2,1)S(1)}, u32[]{:S(2)}, u32[]{:S(2)}) collective-permute-start(bf16[128,512]{1,0:T(8,128)(2,1)S(1)} %pad_maximum_fusion.5), channel_id=1, source_target_pairs={{0,2},{2,0},{4,6},{6,4},{8,10},{10,8},{12,14},{14,12},{1,3},{3,1},... | collective-permute-start | bytes 393224 | tf_op jit(solution)/shard_map/ppermute | solution.py:18
  38.1 0.8 %collective-permute-start.6 = (bf16[128,512]{1,0:T(8,128)(2,1)S(1)}, bf16[128,512]{1,0:T(8,128)(2,1)S(1)}, u32[]{:S(2)}, u32[]{:S(2)}) collective-permute-start(bf16[128,512]{1,0:T(8,128)(2,1)S(1)} %pad_maximum_fusion.3), channel_id=1, source_target_pairs={{0,2},{2,0},{4,6},{6,4},{8,10},{10,8},{12,14},{14,12},{1,3},{3,1},... | collective-permute-start | bytes 393224 | tf_op jit(solution)/shard_map/ppermute | solution.py:18
  39.0 0.6 collective-permute-done.17
  39.6 2.1 %collective-permute-done.15 = bf16[128,512]{1,0:T(8,128)(2,1)S(1)} collective-permute-done((bf16[128,512]{1,0:T(8,128)(2,1)S(1)}, bf16[128,512]{1,0:T(8,128)(2,1)S(1)}, u32[]{:S(2)}, u32[]{:S(2)}) %collective-permute-start.15) | collective-permute-done | bytes 131104 | tf_op jit(solution)/shard_map/ppermute | solution.py:18
  42.2 0.7 collective-permute-done.8
  43.9 0.4 fusion.2.mine_ref
  44.4 1.5 %collective-permute-done.18.other_ref = f32[512,128]{1,0:T(8,128)S(1)} collective-permute-done((f32[512,128]{1,0:T(8,128)S(1)}, f32[512,128]{1,0:T(8,128)S(1)}, u32[]{:S(2)}, u32[]{:S(2)}) %collective-permute-start.18) | collective-permute-done | bytes 262176 | tf_op jit(solution)/shard_map/ppermute | solution.py:18
  46.0 0.5 make_gram.1
  46.4 3.1 %collective-permute-start.22 = (f32[72,128]{1,0:T(8,128)S(1)}, f32[72,128]{1,0:T(8,128)S(1)}, u32[]{:S(2)}, u32[]{:S(2)}) collective-permute-start(f32[72,128]{1,0:T(8,128)S(1)} %make_gram.1), channel_id=1, source_target_pairs={{0,10},{1,15},{2,8},{3,13},{4,14},{5,11},{6,12},{7,9},{8,2},{9,7},... | collective-permute-start | bytes 110600 | tf_op jit(solution)/shard_map/ppermute | solution.py:36
  49.8 1.1 %collective-permute-start.20 = (f32[72,128]{1,0:T(8,128)S(1)}, f32[72,128]{1,0:T(8,128)S(1)}, u32[]{:S(2)}, u32[]{:S(2)}) collective-permute-start(f32[72,128]{1,0:T(8,128)S(1)} %make_gram.1), channel_id=1, source_target_pairs={{0,2},{1,7},{2,0},{3,5},{4,6},{5,3},{6,4},{7,1},{8,10},{9,15},{10,... | collective-permute-start | bytes 110600 | tf_op jit(solution)/shard_map/ppermute | solution.py:36
  50.9 0.7 collective-permute-start.19
  51.6 1.7 %collective-permute-done.22 = f32[72,128]{1,0:T(8,128)S(1)} collective-permute-done((f32[72,128]{1,0:T(8,128)S(1)}, f32[72,128]{1,0:T(8,128)S(1)}, u32[]{:S(2)}, u32[]{:S(2)}) %collective-permute-start.22) | collective-permute-done | bytes 36896 | tf_op jit(solution)/shard_map/ppermute | solution.py:36
  53.3 1.9 %collective-permute-done.21 = f32[72,128]{1,0:T(8,128)S(1)} collective-permute-done((f32[72,128]{1,0:T(8,128)S(1)}, f32[72,128]{1,0:T(8,128)S(1)}, u32[]{:S(2)}, u32[]{:S(2)}) %collective-permute-start.21) | collective-permute-done | bytes 36896 | tf_op jit(solution)/shard_map/ppermute | solution.py:36
  55.6 0.9 %collective-permute-done.23 = f32[72,128]{1,0:T(8,128)S(1)} collective-permute-done((f32[72,128]{1,0:T(8,128)S(1)}, f32[72,128]{1,0:T(8,128)S(1)}, u32[]{:S(2)}, u32[]{:S(2)}) %collective-permute-start.23) | collective-permute-done | bytes 36896 | tf_op jit(solution)/shard_map/ppermute | solution.py:18
  56.5 4.6 %make_basis.1 = (f32[512,128]{1,0:T(8,128)}, f32[128,1024]{1,0:T(8,128)S(1)}, f32[128,1024]{1,0:T(8,128)S(1)}, f32[128,1024]{1,0:T(8,128)S(1)}, f32[128,1024]{1,0:T(8,128)S(1)}) custom-call(f32[72,128]{1,0:T(8,128)S(1)} %add.102.gram_ref, f32[512,128]{1,0:T(8,128)S(1)} %fusion.2.mine_ref, f32[512,128]{1,0:T(8,128)S(1)} %collective-permute-done.18.other_ref, ...), custom_call_target="tpu_custom_call" | custom-call | tf_op jit(solution)/shard_map/make_basis/pallas_call | solution.py:295
  61.2 1.1 %collective-permute-start.24 = (bf16[2,2,16,1024]{3,2,0,1:T(8,128)(2,1)S(1)}, bf16[2,2,16,1024]{3,2,0,1:T(8,128)(2,1)S(1)}, u32[]{:S(2)}, u32[]{:S(2)}) collective-permute-start(bf16[2,2,16,1024]{3,2,0,1:T(8,128)(2,1)S(1)} %fusion.24), channel_id=1, source_target_pairs={{0,2},{2,0},{4,6},{6,4},{8,10},{10,8},{12,14},{14,12},{1,3},{3,1},... | collective-permute-start | bytes 393224 | tf_op jit(solution)/shard_map/ppermute | solution.py:18
  62.4 1.7 %collective-permute-start.26 = (bf16[2,2,16,1024]{3,2,0,1:T(8,128)(2,1)S(1)}, bf16[2,2,16,1024]{3,2,0,1:T(8,128)(2,1)S(1)}, u32[]{:S(2)}, u32[]{:S(2)}) collective-permute-start(bf16[2,2,16,1024]{3,2,0,1:T(8,128)(2,1)S(1)} %fusion.25), channel_id=1, source_target_pairs={{0,4},{2,6},{4,0},{6,2},{8,12},{10,14},{12,8},{14,10},{1,5},{3,7},... | collective-permute-start | bytes 393224 | tf_op jit(solution)/shard_map/ppermute | solution.py:18
  64.1 1.2 %collective-permute-start.29 = (bf16[2,2,16,1024]{3,2,0,1:T(8,128)(2,1)S(1)}, bf16[2,2,16,1024]{3,2,0,1:T(8,128)(2,1)S(1)}, u32[]{:S(2)}, u32[]{:S(2)}) collective-permute-start(bf16[2,2,16,1024]{3,2,0,1:T(8,128)(2,1)S(1)} %fusion.26), channel_id=1, source_target_pairs={{0,2},{2,0},{4,6},{6,4},{8,10},{10,8},{12,14},{14,12},{1,3},{3,1},... | collective-permute-start | bytes 393224 | tf_op jit(solution)/shard_map/ppermute | solution.py:18
  65.7 1.6 %collective-permute-done.24 = bf16[2,2,16,1024]{3,2,0,1:T(8,128)(2,1)S(1)} collective-permute-done((bf16[2,2,16,1024]{3,2,0,1:T(8,128)(2,1)S(1)}, bf16[2,2,16,1024]{3,2,0,1:T(8,128)(2,1)S(1)}, u32[]{:S(2)}, u32[]{:S(2)}) %collective-permute-start.24) | collective-permute-done | bytes 131104 | tf_op jit(solution)/shard_map/ppermute | solution.py:18
  67.4 2.0 %collective-permute-start.25 = (bf16[2,16,1024]{2,1,0:T(8,128)(2,1)S(1)}, bf16[2,16,1024]{2,1,0:T(8,128)(2,1)S(1)}, u32[]{:S(2)}, u32[]{:S(2)}) collective-permute-start(bf16[2,16,1024]{2,1,0:T(8,128)(2,1)S(1)} %fusion.32), channel_id=1, source_target_pairs={{0,4},{2,6},{4,0},{6,2},{8,12},{10,14},{12,8},{14,10},{1,5},{3,7},... | collective-permute-start | bytes 196616 | tf_op jit(solution)/shard_map/ppermute | solution.py:18
  69.5 1.0 %collective-permute-start.27 = (bf16[2,16,1024]{2,1,0:T(8,128)(2,1)S(1)}, bf16[2,16,1024]{2,1,0:T(8,128)(2,1)S(1)}, u32[]{:S(2)}, u32[]{:S(2)}) collective-permute-start(bf16[2,16,1024]{2,1,0:T(8,128)(2,1)S(1)} %fusion.33), channel_id=1, source_target_pairs={{0,2},{2,0},{4,6},{6,4},{8,10},{10,8},{12,14},{14,12},{1,3},{3,1},... | collective-permute-start | bytes 196616 | tf_op jit(solution)/shard_map/ppermute | solution.py:18
  70.6 1.2 %collective-permute-start.30 = (bf16[2,16,1024]{2,1,0:T(8,128)(2,1)S(1)}, bf16[2,16,1024]{2,1,0:T(8,128)(2,1)S(1)}, u32[]{:S(2)}, u32[]{:S(2)}) collective-permute-start(bf16[2,16,1024]{2,1,0:T(8,128)(2,1)S(1)} %fusion.35), channel_id=1, source_target_pairs={{0,4},{2,6},{4,0},{6,2},{8,12},{10,14},{12,8},{14,10},{1,5},{3,7},... | collective-permute-start | bytes 196616 | tf_op jit(solution)/shard_map/ppermute | solution.py:18
  71.9 1.0 %collective-permute-start.32 = (bf16[2,16,1024]{2,1,0:T(8,128)(2,1)S(1)}, bf16[2,16,1024]{2,1,0:T(8,128)(2,1)S(1)}, u32[]{:S(2)}, u32[]{:S(2)}) collective-permute-start(bf16[2,16,1024]{2,1,0:T(8,128)(2,1)S(1)} %fusion.36), channel_id=1, source_target_pairs={{0,2},{2,0},{4,6},{6,4},{8,10},{10,8},{12,14},{14,12},{1,3},{3,1},... | collective-permute-start | bytes 196616 | tf_op jit(solution)/shard_map/ppermute | solution.py:18
  72.9 1.2 %collective-permute-done.27 = bf16[2,16,1024]{2,1,0:T(8,128)(2,1)S(1)} collective-permute-done((bf16[2,16,1024]{2,1,0:T(8,128)(2,1)S(1)}, bf16[2,16,1024]{2,1,0:T(8,128)(2,1)S(1)}, u32[]{:S(2)}, u32[]{:S(2)}) %collective-permute-start.27) | collective-permute-done | bytes 65568 | tf_op jit(solution)/shard_map/ppermute | solution.py:18
  74.1 2.8 %collective-permute-start.28 = (bf16[1,16,2048]{2,1,0:T(8,128)(2,1)S(1)}, bf16[1,16,2048]{2,1,0:T(8,128)(2,1)S(1)}, u32[]{:S(2)}, u32[]{:S(2)}) collective-permute-start(bf16[1,16,2048]{2,1,0:T(8,128)(2,1)S(1)} %fusion.34), channel_id=1, source_target_pairs={{0,8},{2,10},{4,12},{6,14},{8,0},{10,2},{12,4},{14,6},{1,9},{3,11}... | collective-permute-start | bytes 196616 | tf_op jit(solution)/shard_map/ppermute | solution.py:18
  77.1 2.0 %collective-permute-start.33 = (bf16[1,16,2048]{2,1,0:T(8,128)(2,1)S(1)}, bf16[1,16,2048]{2,1,0:T(8,128)(2,1)S(1)}, u32[]{:S(2)}, u32[]{:S(2)}) collective-permute-start(bf16[1,16,2048]{2,1,0:T(8,128)(2,1)S(1)} %fusion.37), channel_id=1, source_target_pairs={{0,8},{2,10},{4,12},{6,14},{8,0},{10,2},{12,4},{14,6},{1,9},{3,11}... | collective-permute-start | bytes 196616 | tf_op jit(solution)/shard_map/ppermute | solution.py:18
  79.1 2.0 %collective-permute-done.28 = bf16[1,16,2048]{2,1,0:T(8,128)(2,1)S(1)} collective-permute-done((bf16[1,16,2048]{2,1,0:T(8,128)(2,1)S(1)}, bf16[1,16,2048]{2,1,0:T(8,128)(2,1)S(1)}, u32[]{:S(2)}, u32[]{:S(2)}) %collective-permute-start.28) | collective-permute-done | bytes 65568 | tf_op jit(solution)/shard_map/ppermute | solution.py:18
  81.1 1.9 %collective-permute-done.33 = bf16[1,16,2048]{2,1,0:T(8,128)(2,1)S(1)} collective-permute-done((bf16[1,16,2048]{2,1,0:T(8,128)(2,1)S(1)}, bf16[1,16,2048]{2,1,0:T(8,128)(2,1)S(1)}, u32[]{:S(2)}, u32[]{:S(2)}) %collective-permute-start.33) | collective-permute-done | bytes 65568 | tf_op jit(solution)/shard_map/ppermute | solution.py:18
  83.0 0.7 pad_maximum_fusion.2
  (91 shorter events, 4.8 us)
Async XLA Ops:
  0.6 0.9 %copy-start = (bf16[512,128]{1,0:T(8,128)(2,1)S(1)}, bf16[512,128]{1,0:T(8,128)(2,1)}, u32[]{:S(2)}) copy-start(bf16[512,128]{1,0:T(8,128)(2,1)} %start_ref.1) | copy-start | bytes 393220
  4.6 7.0 %collective-permute-start.11 = (bf16[128,512]{1,0:T(8,128)(2,1)S(1)}, bf16[128,512]{1,0:T(8,128)(2,1)S(1)}, u32[]{:S(2)}, u32[]{:S(2)}) collective-permute-start(bf16[128,512]{1,0:T(8,128)(2,1)S(1)} %select_convert_fusion.4), channel_id=1, source_target_pairs={{0,4},{2,6},{4,0},{6,2},{8,12},{10,14},{12,8},{14,10},{1,5},{3,7},... | collective-permute-start | bytes 393224 | tf_op jit(solution)/shard_map/ppermute | solution.py:18
  7.7 6.3 %collective-permute-start.9 = (bf16[128,512]{1,0:T(8,128)(2,1)S(1)}, bf16[128,512]{1,0:T(8,128)(2,1)S(1)}, u32[]{:S(2)}, u32[]{:S(2)}) collective-permute-start(bf16[128,512]{1,0:T(8,128)(2,1)S(1)} %select_convert_fusion.5), channel_id=1, source_target_pairs={{0,2},{2,0},{4,6},{6,4},{8,10},{10,8},{12,14},{14,12},{1,3},{3,1},... | collective-permute-start | bytes 393224 | tf_op jit(solution)/shard_map/ppermute | solution.py:18
  9.3 6.6 %collective-permute-start.2 = (bf16[128,512]{1,0:T(8,128)(2,1)S(1)}, bf16[128,512]{1,0:T(8,128)(2,1)S(1)}, u32[]{:S(2)}, u32[]{:S(2)}) collective-permute-start(bf16[128,512]{1,0:T(8,128)(2,1)S(1)} %select_convert_fusion.6), channel_id=1, source_target_pairs={{0,4},{2,6},{4,0},{6,2},{8,12},{10,14},{12,8},{14,10},{1,5},{3,7},... | collective-permute-start | bytes 393224 | tf_op jit(solution)/shard_map/ppermute | solution.py:18
  9.8 6.7 %collective-permute-start = (bf16[128,512]{1,0:T(8,128)(2,1)S(1)}, bf16[128,512]{1,0:T(8,128)(2,1)S(1)}, u32[]{:S(2)}, u32[]{:S(2)}) collective-permute-start(bf16[128,512]{1,0:T(8,128)(2,1)S(1)} %select_convert_fusion.7), channel_id=1, source_target_pairs={{0,2},{2,0},{4,6},{6,4},{8,10},{10,8},{12,14},{14,12},{1,3},{3,1},... | collective-permute-start | bytes 393224 | tf_op jit(solution)/shard_map/ppermute | solution.py:18
  11.7 6.5 %collective-permute-start.12 = (bf16[128,256]{1,0:T(8,128)(2,1)S(1)}, bf16[128,256]{1,0:T(8,128)(2,1)S(1)}, u32[]{:S(2)}, u32[]{:S(2)}) collective-permute-start(bf16[128,256]{1,0:T(8,128)(2,1)S(1)} %select_convert_fusion.14), channel_id=1, source_target_pairs={{0,2},{2,0},{4,6},{6,4},{8,10},{10,8},{12,14},{14,12},{1,3},{3,1},... | collective-permute-start | bytes 196616 | tf_op jit(solution)/shard_map/ppermute | solution.py:18
  14.1 4.6 %collective-permute-start.10 = (bf16[128,256]{1,0:T(8,128)(2,1)S(1)}, bf16[128,256]{1,0:T(8,128)(2,1)S(1)}, u32[]{:S(2)}, u32[]{:S(2)}) collective-permute-start(bf16[128,256]{1,0:T(8,128)(2,1)S(1)} %select_convert_fusion.15), channel_id=1, source_target_pairs={{0,4},{2,6},{4,0},{6,2},{8,12},{10,14},{12,8},{14,10},{1,5},{3,7},... | collective-permute-start | bytes 196616 | tf_op jit(solution)/shard_map/ppermute | solution.py:18
  15.9 25.8 %copy-start.1 = (bf16[512,4096]{1,0:T(8,128)(2,1)S(1)}, bf16[512,4096]{1,0:T(8,128)(2,1)}, u32[]{:S(2)}) copy-start(bf16[512,4096]{1,0:T(8,128)(2,1)} %slab_ref.3) | copy-start | bytes 12582916
  16.0 5.8 %collective-permute-start.3 = (bf16[128,256]{1,0:T(8,128)(2,1)S(1)}, bf16[128,256]{1,0:T(8,128)(2,1)S(1)}, u32[]{:S(2)}, u32[]{:S(2)}) collective-permute-start(bf16[128,256]{1,0:T(8,128)(2,1)S(1)} %select_convert_fusion.16), channel_id=1, source_target_pairs={{0,2},{2,0},{4,6},{6,4},{8,10},{10,8},{12,14},{14,12},{1,3},{3,1},... | collective-permute-start | bytes 196616 | tf_op jit(solution)/shard_map/ppermute | solution.py:18
  16.7 5.1 %collective-permute-start.1 = (bf16[128,256]{1,0:T(8,128)(2,1)S(1)}, bf16[128,256]{1,0:T(8,128)(2,1)S(1)}, u32[]{:S(2)}, u32[]{:S(2)}) collective-permute-start(bf16[128,256]{1,0:T(8,128)(2,1)S(1)} %select_convert_fusion.17), channel_id=1, source_target_pairs={{0,4},{2,6},{4,0},{6,2},{8,12},{10,14},{12,8},{14,10},{1,5},{3,7},... | collective-permute-start | bytes 196616 | tf_op jit(solution)/shard_map/ppermute | solution.py:18
  18.8 10.7 %collective-permute-start.13 = (bf16[128,512]{1,0:T(8,128)(2,1)S(1)}, bf16[128,512]{1,0:T(8,128)(2,1)S(1)}, u32[]{:S(2)}, u32[]{:S(2)}) collective-permute-start(bf16[128,512]{1,0:T(8,128)(2,1)S(1)} %fusion.22), channel_id=1, source_target_pairs={{0,8},{2,10},{4,12},{6,14},{8,0},{10,2},{12,4},{14,6},{1,9},{3,11}... | collective-permute-start | bytes 393224 | tf_op jit(solution)/shard_map/ppermute | solution.py:18
  21.9 8.9 %collective-permute-start.4 = (bf16[128,512]{1,0:T(8,128)(2,1)S(1)}, bf16[128,512]{1,0:T(8,128)(2,1)S(1)}, u32[]{:S(2)}, u32[]{:S(2)}) collective-permute-start(bf16[128,512]{1,0:T(8,128)(2,1)S(1)} %fusion.23), channel_id=1, source_target_pairs={{0,8},{2,10},{4,12},{6,14},{8,0},{10,2},{12,4},{14,6},{1,9},{3,11}... | collective-permute-start | bytes 393224 | tf_op jit(solution)/shard_map/ppermute | solution.py:18
  29.5 5.0 %collective-permute-start.14 = (bf16[128,256]{1,0:T(8,128)(2,1)S(1)}, bf16[128,256]{1,0:T(8,128)(2,1)S(1)}, u32[]{:S(2)}, u32[]{:S(2)}) collective-permute-start(bf16[128,256]{1,0:T(8,128)(2,1)S(1)} %get-tuple-element.50), channel_id=1, source_target_pairs={{0,4},{2,6},{4,0},{6,2},{8,12},{10,14},{12,8},{14,10},{1,5},{3,7},... | collective-permute-start | bytes 196616 | tf_op jit(solution)/shard_map/ppermute | solution.py:18
  29.7 4.7 %collective-permute-start.16 = (bf16[128,256]{1,0:T(8,128)(2,1)S(1)}, bf16[128,256]{1,0:T(8,128)(2,1)S(1)}, u32[]{:S(2)}, u32[]{:S(2)}) collective-permute-start(bf16[128,256]{1,0:T(8,128)(2,1)S(1)} %get-tuple-element.51), channel_id=1, source_target_pairs={{0,2},{2,0},{4,6},{6,4},{8,10},{10,8},{12,14},{14,12},{1,3},{3,1},... | collective-permute-start | bytes 196616 | tf_op jit(solution)/shard_map/ppermute | solution.py:18
  30.9 7.0 %collective-permute-start.5 = (bf16[128,256]{1,0:T(8,128)(2,1)S(1)}, bf16[128,256]{1,0:T(8,128)(2,1)S(1)}, u32[]{:S(2)}, u32[]{:S(2)}) collective-permute-start(bf16[128,256]{1,0:T(8,128)(2,1)S(1)} %get-tuple-element.46), channel_id=1, source_target_pairs={{0,4},{2,6},{4,0},{6,2},{8,12},{10,14},{12,8},{14,10},{1,5},{3,7},... | collective-permute-start | bytes 196616 | tf_op jit(solution)/shard_map/ppermute | solution.py:18
  32.8 5.0 %collective-permute-start.7 = (bf16[128,256]{1,0:T(8,128)(2,1)S(1)}, bf16[128,256]{1,0:T(8,128)(2,1)S(1)}, u32[]{:S(2)}, u32[]{:S(2)}) collective-permute-start(bf16[128,256]{1,0:T(8,128)(2,1)S(1)} %get-tuple-element.47), channel_id=1, source_target_pairs={{0,2},{2,0},{4,6},{6,4},{8,10},{10,8},{12,14},{14,12},{1,3},{3,1},... | collective-permute-start | bytes 196616 | tf_op jit(solution)/shard_map/ppermute | solution.py:18
  34.5 5.1 %collective-permute-start.17 = (bf16[128,512]{1,0:T(8,128)(2,1)S(1)}, bf16[128,512]{1,0:T(8,128)(2,1)S(1)}, u32[]{:S(2)}, u32[]{:S(2)}) collective-permute-start(bf16[128,512]{1,0:T(8,128)(2,1)S(1)} %pad_maximum_fusion.6), channel_id=1, source_target_pairs={{0,4},{2,6},{4,0},{6,2},{8,12},{10,14},{12,8},{14,10},{1,5},{3,7},... | collective-permute-start | bytes 393224 | tf_op jit(solution)/shard_map/ppermute | solution.py:18
  36.7 5.0 %collective-permute-start.15 = (bf16[128,512]{1,0:T(8,128)(2,1)S(1)}, bf16[128,512]{1,0:T(8,128)(2,1)S(1)}, u32[]{:S(2)}, u32[]{:S(2)}) collective-permute-start(bf16[128,512]{1,0:T(8,128)(2,1)S(1)} %pad_maximum_fusion.5), channel_id=1, source_target_pairs={{0,2},{2,0},{4,6},{6,4},{8,10},{10,8},{12,14},{14,12},{1,3},{3,1},... | collective-permute-start | bytes 393224 | tf_op jit(solution)/shard_map/ppermute | solution.py:18
  37.9 5.0 %collective-permute-start.8 = (bf16[128,512]{1,0:T(8,128)(2,1)S(1)}, bf16[128,512]{1,0:T(8,128)(2,1)S(1)}, u32[]{:S(2)}, u32[]{:S(2)}) collective-permute-start(bf16[128,512]{1,0:T(8,128)(2,1)S(1)} %pad_maximum_fusion.4), channel_id=1, source_target_pairs={{0,4},{2,6},{4,0},{6,2},{8,12},{10,14},{12,8},{14,10},{1,5},{3,7},... | collective-permute-start | bytes 393224 | tf_op jit(solution)/shard_map/ppermute | solution.py:18
  38.1 5.7 %collective-permute-start.6 = (bf16[128,512]{1,0:T(8,128)(2,1)S(1)}, bf16[128,512]{1,0:T(8,128)(2,1)S(1)}, u32[]{:S(2)}, u32[]{:S(2)}) collective-permute-start(bf16[128,512]{1,0:T(8,128)(2,1)S(1)} %pad_maximum_fusion.3), channel_id=1, source_target_pairs={{0,2},{2,0},{4,6},{6,4},{8,10},{10,8},{12,14},{14,12},{1,3},{3,1},... | collective-permute-start | bytes 393224 | tf_op jit(solution)/shard_map/ppermute | solution.py:18
  44.3 1.6 %collective-permute-start.18 = (f32[512,128]{1,0:T(8,128)S(1)}, f32[512,128]{1,0:T(8,128)S(1)}, u32[]{:S(2)}, u32[]{:S(2)}) collective-permute-start(f32[512,128]{1,0:T(8,128)S(1)} %fusion.2.mine_ref), channel_id=1, source_target_pairs={{0,1},{1,0},{2,3},{3,2},{4,5},{5,4},{6,7},{7,6},{8,9},{9,8},{10,11... | collective-permute-start | bytes 786440 | tf_op jit(solution)/shard_map/ppermute | solution.py:18
  46.4 6.8 %collective-permute-start.22 = (f32[72,128]{1,0:T(8,128)S(1)}, f32[72,128]{1,0:T(8,128)S(1)}, u32[]{:S(2)}, u32[]{:S(2)}) collective-permute-start(f32[72,128]{1,0:T(8,128)S(1)} %make_gram.1), channel_id=1, source_target_pairs={{0,10},{1,15},{2,8},{3,13},{4,14},{5,11},{6,12},{7,9},{8,2},{9,7},... | collective-permute-start | bytes 110600 | tf_op jit(solution)/shard_map/ppermute | solution.py:36
  49.5 5.6 %collective-permute-start.21 = (f32[72,128]{1,0:T(8,128)S(1)}, f32[72,128]{1,0:T(8,128)S(1)}, u32[]{:S(2)}, u32[]{:S(2)}) collective-permute-start(f32[72,128]{1,0:T(8,128)S(1)} %make_gram.1), channel_id=1, source_target_pairs={{0,8},{1,13},{2,10},{3,15},{4,12},{5,9},{6,14},{7,11},{8,0},{9,5},... | collective-permute-start | bytes 110600 | tf_op jit(solution)/shard_map/ppermute | solution.py:36
  49.8 5.4 %collective-permute-start.20 = (f32[72,128]{1,0:T(8,128)S(1)}, f32[72,128]{1,0:T(8,128)S(1)}, u32[]{:S(2)}, u32[]{:S(2)}) collective-permute-start(f32[72,128]{1,0:T(8,128)S(1)} %make_gram.1), channel_id=1, source_target_pairs={{0,2},{1,7},{2,0},{3,5},{4,6},{5,3},{6,4},{7,1},{8,10},{9,15},{10,... | collective-permute-start | bytes 110600 | tf_op jit(solution)/shard_map/ppermute | solution.py:36
  50.9 4.3 %collective-permute-start.19 = (f32[72,128]{1,0:T(8,128)S(1)}, f32[72,128]{1,0:T(8,128)S(1)}, u32[]{:S(2)}, u32[]{:S(2)}) collective-permute-start(f32[72,128]{1,0:T(8,128)S(1)} %make_gram.1), channel_id=1, source_target_pairs={{1,5},{3,7},{5,1},{7,3},{9,13},{11,15},{13,9},{15,11},{17,21},{19,... | collective-permute-start | bytes 110600 | tf_op jit(solution)/shard_map/ppermute | solution.py:36
  55.2 1.3 %collective-permute-start.23 = (f32[72,128]{1,0:T(8,128)S(1)}, f32[72,128]{1,0:T(8,128)S(1)}, u32[]{:S(2)}, u32[]{:S(2)}) collective-permute-start(f32[72,128]{1,0:T(8,128)S(1)} %add_add_fusion), channel_id=1, source_target_pairs={{0,1},{1,0},{2,3},{3,2},{4,5},{5,4},{6,7},{7,6},{8,9},{9,8},{10,11... | collective-permute-start | bytes 110600 | tf_op jit(solution)/shard_map/ppermute | solution.py:18
  61.2 6.1 %collective-permute-start.24 = (bf16[2,2,16,1024]{3,2,0,1:T(8,128)(2,1)S(1)}, bf16[2,2,16,1024]{3,2,0,1:T(8,128)(2,1)S(1)}, u32[]{:S(2)}, u32[]{:S(2)}) collective-permute-start(bf16[2,2,16,1024]{3,2,0,1:T(8,128)(2,1)S(1)} %fusion.24), channel_id=1, source_target_pairs={{0,2},{2,0},{4,6},{6,4},{8,10},{10,8},{12,14},{14,12},{1,3},{3,1},... | collective-permute-start | bytes 393224 | tf_op jit(solution)/shard_map/ppermute | solution.py:18
  62.4 7.1 %collective-permute-start.26 = (bf16[2,2,16,1024]{3,2,0,1:T(8,128)(2,1)S(1)}, bf16[2,2,16,1024]{3,2,0,1:T(8,128)(2,1)S(1)}, u32[]{:S(2)}, u32[]{:S(2)}) collective-permute-start(bf16[2,2,16,1024]{3,2,0,1:T(8,128)(2,1)S(1)} %fusion.25), channel_id=1, source_target_pairs={{0,4},{2,6},{4,0},{6,2},{8,12},{10,14},{12,8},{14,10},{1,5},{3,7},... | collective-permute-start | bytes 393224 | tf_op jit(solution)/shard_map/ppermute | solution.py:18
  64.1 6.4 %collective-permute-start.29 = (bf16[2,2,16,1024]{3,2,0,1:T(8,128)(2,1)S(1)}, bf16[2,2,16,1024]{3,2,0,1:T(8,128)(2,1)S(1)}, u32[]{:S(2)}, u32[]{:S(2)}) collective-permute-start(bf16[2,2,16,1024]{3,2,0,1:T(8,128)(2,1)S(1)} %fusion.26), channel_id=1, source_target_pairs={{0,2},{2,0},{4,6},{6,4},{8,10},{10,8},{12,14},{14,12},{1,3},{3,1},... | collective-permute-start | bytes 393224 | tf_op jit(solution)/shard_map/ppermute | solution.py:18
  65.4 6.4 %collective-permute-start.31 = (bf16[2,2,16,1024]{3,2,0,1:T(8,128)(2,1)S(1)}, bf16[2,2,16,1024]{3,2,0,1:T(8,128)(2,1)S(1)}, u32[]{:S(2)}, u32[]{:S(2)}) collective-permute-start(bf16[2,2,16,1024]{3,2,0,1:T(8,128)(2,1)S(1)} %fusion.27), channel_id=1, source_target_pairs={{0,4},{2,6},{4,0},{6,2},{8,12},{10,14},{12,8},{14,10},{1,5},{3,7},... | collective-permute-start | bytes 393224 | tf_op jit(solution)/shard_map/ppermute | solution.py:18
  67.4 5.4 %collective-permute-start.25 = (bf16[2,16,1024]{2,1,0:T(8,128)(2,1)S(1)}, bf16[2,16,1024]{2,1,0:T(8,128)(2,1)S(1)}, u32[]{:S(2)}, u32[]{:S(2)}) collective-permute-start(bf16[2,16,1024]{2,1,0:T(8,128)(2,1)S(1)} %fusion.32), channel_id=1, source_target_pairs={{0,4},{2,6},{4,0},{6,2},{8,12},{10,14},{12,8},{14,10},{1,5},{3,7},... | collective-permute-start | bytes 196616 | tf_op jit(solution)/shard_map/ppermute | solution.py:18
  69.5 4.6 %collective-permute-start.27 = (bf16[2,16,1024]{2,1,0:T(8,128)(2,1)S(1)}, bf16[2,16,1024]{2,1,0:T(8,128)(2,1)S(1)}, u32[]{:S(2)}, u32[]{:S(2)}) collective-permute-start(bf16[2,16,1024]{2,1,0:T(8,128)(2,1)S(1)} %fusion.33), channel_id=1, source_target_pairs={{0,2},{2,0},{4,6},{6,4},{8,10},{10,8},{12,14},{14,12},{1,3},{3,1},... | collective-permute-start | bytes 196616 | tf_op jit(solution)/shard_map/ppermute | solution.py:18
  70.6 6.4 %collective-permute-start.30 = (bf16[2,16,1024]{2,1,0:T(8,128)(2,1)S(1)}, bf16[2,16,1024]{2,1,0:T(8,128)(2,1)S(1)}, u32[]{:S(2)}, u32[]{:S(2)}) collective-permute-start(bf16[2,16,1024]{2,1,0:T(8,128)(2,1)S(1)} %fusion.35), channel_id=1, source_target_pairs={{0,4},{2,6},{4,0},{6,2},{8,12},{10,14},{12,8},{14,10},{1,5},{3,7},... | collective-permute-start | bytes 196616 | tf_op jit(solution)/shard_map/ppermute | solution.py:18
  71.9 5.1 %collective-permute-start.32 = (bf16[2,16,1024]{2,1,0:T(8,128)(2,1)S(1)}, bf16[2,16,1024]{2,1,0:T(8,128)(2,1)S(1)}, u32[]{:S(2)}, u32[]{:S(2)}) collective-permute-start(bf16[2,16,1024]{2,1,0:T(8,128)(2,1)S(1)} %fusion.36), channel_id=1, source_target_pairs={{0,2},{2,0},{4,6},{6,4},{8,10},{10,8},{12,14},{14,12},{1,3},{3,1},... | collective-permute-start | bytes 196616 | tf_op jit(solution)/shard_map/ppermute | solution.py:18
  74.1 7.0 %collective-permute-start.28 = (bf16[1,16,2048]{2,1,0:T(8,128)(2,1)S(1)}, bf16[1,16,2048]{2,1,0:T(8,128)(2,1)S(1)}, u32[]{:S(2)}, u32[]{:S(2)}) collective-permute-start(bf16[1,16,2048]{2,1,0:T(8,128)(2,1)S(1)} %fusion.34), channel_id=1, source_target_pairs={{0,8},{2,10},{4,12},{6,14},{8,0},{10,2},{12,4},{14,6},{1,9},{3,11}... | collective-permute-start | bytes 196616 | tf_op jit(solution)/shard_map/ppermute | solution.py:18
  77.1 5.9 %collective-permute-start.33 = (bf16[1,16,2048]{2,1,0:T(8,128)(2,1)S(1)}, bf16[1,16,2048]{2,1,0:T(8,128)(2,1)S(1)}, u32[]{:S(2)}, u32[]{:S(2)}) collective-permute-start(bf16[1,16,2048]{2,1,0:T(8,128)(2,1)S(1)} %fusion.37), channel_id=1, source_target_pairs={{0,8},{2,10},{4,12},{6,14},{8,0},{10,2},{12,4},{14,6},{1,9},{3,11}... | collective-permute-start | bytes 196616 | tf_op jit(solution)/shard_map/ppermute | solution.py:18

commit v18 on v15

--- a/solution.py
+++ b/solution.py
@@ -8,7 +8,7 @@
 from jax.experimental.pallas import tpu as pltpu
 from jax.sharding import PartitionSpec as P
 
-CHUNKS = 4
+CHUNKS = (1, 1, 3, 3)
 TILE = 512
 KERNEL_VMEM = 50 * 2**20
 
@@ -100,29 +100,46 @@
     return copies
 
 
+def store(outs, start, tile):
+    for out in outs:
+        if start < out.shape[1]:
+            out[:, start : start + TILE] = tile
+            return
+        start -= out.shape[1]
+
+
+def widths_of(cols):
+    return [cols // sum(CHUNKS) * part for part in CHUNKS]
+
+
 def sketch_kernel(start_ref, slab_ref, *refs):
     outs, (buffer, arrived) = refs[:-2], refs[-2:]
     copies = fetch_tiles(slab_ref, buffer, arrived)
     left = start_ref[...].T
     for tile, copy in enumerate(copies):
         copy.wait()
-        out, inner = divmod(tile * TILE, outs[0].shape[1])
-        outs[out][:, inner : inner + TILE] = lax.dot_general(
-            left, buffer[tile], (((1,), (0,)), ((), ())), preferred_element_type=jnp.float32
-        )
-
-
-def first_product(start, slab, chunks):
+        store(
+            outs,
+            tile * TILE,
+            lax.dot_general(
+                left, buffer[tile], (((1,), (0,)), ((), ())), preferred_element_type=jnp.float32
+            ),
+        )
+
+
+def first_product(start, slab):
     rows, width = start.shape
     cols = slab.shape[1]
     return pl.pallas_call(
         sketch_kernel,
-        out_shape=[jax.ShapeDtypeStruct((width, cols // chunks), jnp.float32)] * chunks,
+        out_shape=[
+            jax.ShapeDtypeStruct((width, part), jnp.float32) for part in widths_of(cols)
+        ],
         in_specs=[
             pl.BlockSpec(memory_space=pltpu.VMEM),
             pl.BlockSpec(memory_space=pl.ANY),
         ],
-        out_specs=[pl.BlockSpec(memory_space=pltpu.VMEM)] * chunks,
+        out_specs=[pl.BlockSpec(memory_space=pltpu.VMEM)] * len(CHUNKS),
         scratch_shapes=[
             pltpu.VMEM((cols // TILE, rows, TILE), jnp.bfloat16),
             pltpu.SemaphoreType.DMA((cols // TILE,)),
@@ -268,20 +285,19 @@
             (((1,), (0,)), ((), ())),
             preferred_element_type=jnp.float32,
         )
-        out, inner = divmod(start, products[0].shape[1])
-        products[out][:, inner : inner + TILE] = both[:width] + both[width:]
-
-
-def make_basis(gram, mine, other, slab, total_cols, root_rows, chunks):
+        store(products, start, both[:width] + both[width:])
+
+
+def make_basis(gram, mine, other, slab, total_cols, root_rows):
     rows, width = mine.shape
     cols = slab.shape[1]
     return pl.pallas_call(
         functools.partial(basis_kernel, total_cols, root_rows),
         out_shape=[jax.ShapeDtypeStruct((rows, width), jnp.float32)]
-        + [jax.ShapeDtypeStruct((width, cols // chunks), jnp.float32)] * chunks,
+        + [jax.ShapeDtypeStruct((width, part), jnp.float32) for part in widths_of(cols)],
         in_specs=[pl.BlockSpec(memory_space=pltpu.VMEM)] * 3
         + [pl.BlockSpec(memory_space=pl.ANY)],
-        out_specs=[pl.BlockSpec(memory_space=pltpu.VMEM)] * (1 + chunks),
+        out_specs=[pl.BlockSpec(memory_space=pltpu.VMEM)] * (1 + len(CHUNKS)),
         scratch_shapes=[
             pltpu.VMEM((width, width), jnp.float32),
             pltpu.VMEM((width, width), jnp.float32),
@@ -301,13 +317,14 @@
     total_cols = cols_here * lax.axis_size("col")
     root_rows = math.sqrt(total_rows)
 
-    local_cols = first_product(start_sketch, activations, CHUNKS)
+    local_cols = first_product(start_sketch, activations)
     partial_sketch = 0.0
     orders = orders_of("row")
-    step = cols_here // CHUNKS
-    for c in range(CHUNKS):
-        span = slice(c * step, (c + 1) * step)
-        shared = sum_and_share(local_cols[c], "row", orders[c % 2], 1.0 / root_rows)
+    begin = 0
+    for c, local in enumerate(local_cols):
+        span = slice(begin, begin + local.shape[1])
+        begin = span.stop
+        shared = sum_and_share(local, "row", orders[c % 2], 1.0 / root_rows)
         partial_sketch = partial_sketch + lax.dot_general(
             activations[:, span],
             shared,
@@ -317,7 +334,7 @@
     other_sketch = swap(partial_sketch, "col", 1)
     gram = row_sum(make_gram(partial_sketch, other_sketch, total_cols))
     basis, *products = make_basis(
-        gram, partial_sketch, other_sketch, activations, total_cols, root_rows, CHUNKS
+        gram, partial_sketch, other_sketch, activations, total_cols, root_rows
     )
 
     pieces = [

time: 82.8 us -> 102 us (1.23)
  waiting for transfers between devices: 19.5 us -> 39.4 us
    ppermute x34, waiting for transfers between devices: 17 us -> 36.7 us  [swap(): return lax.ppermute(value, axis, [(i, i ^ distance) for i in range(size)])]
  transfers between devices with their start and end apart: 38 -> 38, of which waited for: 18 -> 25; matrix products, arithmetic and copies ran while one was open for 3% -> 2% of each run, Pallas kernels for 0% -> 0%
where the time goes in v18:
time: 102 us
  starting transfers between devices  48.4 us (47%)
  waiting for transfers between devices  39.4 us (39%)
  Pallas kernels  8.12 us (8%)
  other arithmetic  2.13 us (2%)
  matrix products  1.73 us (2%)
  between operations  1.1 us (1%)
  local copies, waits for them, and re-layouts  1.07 us (1%)
    ppermute x34, starting transfers between devices, swap(): return lax.ppermute(value, axis, [(i, i ^ distance) for i in range(size)])  43.3 us
    ppermute x34, waiting for transfers between devices, swap(): return lax.ppermute(value, axis, [(i, i ^ distance) for i in range(size)])  36.7 us
    ppermute x4, starting transfers between devices, row_sum(): terms.append(lax.ppermute(value, ('row', 'col'), pairs))  5.1 us
    pallas_call x1, Pallas kernels, make_basis(): pl.pallas_call(functools.partial(basis_kernel, total_cols, root_rows), ou...  4.63 us
    pallas_call x1, Pallas kernels, first_product(): pl.pallas_call(sketch_kernel, out_shape=[jax.ShapeDtypeStruct((width, par...  2.99 us
    ppermute x4, waiting for transfers between devices, row_sum(): terms.append(lax.ppermute(value, ('row', 'col'), pairs))  2.67 us
  transfers between devices with their start and end apart: 38, of which 25 were waited for; matrix products, arithmetic and copies ran while one was open for 2% of the time, Pallas kernels for 0%

profile of v18, /device:TPU:0, one launch (start us, length us, event | category | flops | bytes accessed | tf_op | source)
XLA Modules:
  0.0 101.9 jit_solution(16163391293984113011)
XLA Ops:
  0.7 0.9 copy-done
  1.6 3.0 %first_product.1 = (f32[128,512]{1,0:T(8,128)S(1)}, f32[128,512]{1,0:T(8,128)S(1)}, f32[128,1536]{1,0:T(8,128)S(1)}, f32[128,1536]{1,0:T(8,128)S(1)}) custom-call(bf16[512,128]{1,0:T(8,128)(2,1)S(1)} %copy-done, bf16[512,4096]{1,0:T(8,128)(2,1)} %slab_ref.3), custom_call_target="tpu_custom_call" | custom-call | flops 536870912 | bytes 4194304 | tf_op jit(solution)/shard_map/first_product/pallas_call | solution.py:133
  4.6 3.1 %collective-permute-start.5 = (bf16[128,256]{1,0:T(8,128)(2,1)S(1)}, bf16[128,256]{1,0:T(8,128)(2,1)S(1)}, u32[]{:S(2)}, u32[]{:S(2)}) collective-permute-start(bf16[128,256]{1,0:T(8,128)(2,1)S(1)} %select_convert_fusion.10), channel_id=1, source_target_pairs={{0,4},{2,6},{4,0},{6,2},{8,12},{10,14},{12,8},{14,10},{1,5},{3,7},... | collective-permute-start | bytes 196616 | tf_op jit(solution)/shard_map/ppermute | solution.py:18
  7.7 1.6 %collective-permute-start = (bf16[128,256]{1,0:T(8,128)(2,1)S(1)}, bf16[128,256]{1,0:T(8,128)(2,1)S(1)}, u32[]{:S(2)}, u32[]{:S(2)}) collective-permute-start(bf16[128,256]{1,0:T(8,128)(2,1)S(1)} %select_convert_fusion.11), channel_id=1, source_target_pairs={{0,2},{2,0},{4,6},{6,4},{8,10},{10,8},{12,14},{14,12},{1,3},{3,1},... | collective-permute-start | bytes 196616 | tf_op jit(solution)/shard_map/ppermute | solution.py:18
  10.1 2.0 %collective-permute-start.6 = (bf16[128,128]{1,0:T(8,128)(2,1)S(1)}, bf16[128,128]{1,0:T(8,128)(2,1)S(1)}, u32[]{:S(2)}, u32[]{:S(2)}) collective-permute-start(bf16[128,128]{1,0:T(8,128)(2,1)S(1)} %select_convert_fusion.16), channel_id=1, source_target_pairs={{0,2},{2,0},{4,6},{6,4},{8,10},{10,8},{12,14},{14,12},{1,3},{3,1},... | collective-permute-start | bytes 98312 | tf_op jit(solution)/shard_map/ppermute | solution.py:18
  12.6 1.8 %collective-permute-start.1 = (bf16[128,128]{1,0:T(8,128)(2,1)S(1)}, bf16[128,128]{1,0:T(8,128)(2,1)S(1)}, u32[]{:S(2)}, u32[]{:S(2)}) collective-permute-start(bf16[128,128]{1,0:T(8,128)(2,1)S(1)} %select_convert_fusion.17), channel_id=1, source_target_pairs={{0,4},{2,6},{4,0},{6,2},{8,12},{10,14},{12,8},{14,10},{1,5},{3,7},... | collective-permute-start | bytes 98312 | tf_op jit(solution)/shard_map/ppermute | solution.py:18
  14.4 2.6 %collective-permute-done.6 = bf16[128,128]{1,0:T(8,128)(2,1)S(1)} collective-permute-done((bf16[128,128]{1,0:T(8,128)(2,1)S(1)}, bf16[128,128]{1,0:T(8,128)(2,1)S(1)}, u32[]{:S(2)}, u32[]{:S(2)}) %collective-permute-start.6) | collective-permute-done | bytes 32800 | tf_op jit(solution)/shard_map/ppermute | solution.py:18
  16.9 2.7 %collective-permute-start.7 = (bf16[128,128]{1,0:T(8,128)(2,1)S(1)}, bf16[128,128]{1,0:T(8,128)(2,1)S(1)}, u32[]{:S(2)}, u32[]{:S(2)}) collective-permute-start(bf16[128,128]{1,0:T(8,128)(2,1)S(1)} %fusion.41), channel_id=1, source_target_pairs={{0,8},{2,10},{4,12},{6,14},{8,0},{10,2},{12,4},{14,6},{1,9},{3,11}... | collective-permute-start | bytes 98312 | tf_op jit(solution)/shard_map/ppermute | solution.py:18
  20.0 2.8 %collective-permute-done.7 = bf16[128,128]{1,0:T(8,128)(2,1)S(1)} collective-permute-done((bf16[128,128]{1,0:T(8,128)(2,1)S(1)}, bf16[128,128]{1,0:T(8,128)(2,1)S(1)}, u32[]{:S(2)}, u32[]{:S(2)}) %collective-permute-start.7) | collective-permute-done | bytes 32800 | tf_op jit(solution)/shard_map/ppermute | solution.py:18
  24.5 1.4 %collective-permute-start.3 = (bf16[128,128]{1,0:T(8,128)(2,1)S(1)}, bf16[128,128]{1,0:T(8,128)(2,1)S(1)}, u32[]{:S(2)}, u32[]{:S(2)}) collective-permute-start(bf16[128,128]{1,0:T(8,128)(2,1)S(1)} %multiply_convert_fusion.3), channel_id=1, source_target_pairs={{0,4},{2,6},{4,0},{6,2},{8,12},{10,14},{12,8},{14,10},{1,5},{3,7},... | collective-permute-start | bytes 98312 | tf_op jit(solution)/shard_map/ppermute | solution.py:18
  25.9 1.0 collective-permute-done.8
  27.0 1.5 %collective-permute-done.3 = bf16[128,128]{1,0:T(8,128)(2,1)S(1)} collective-permute-done((bf16[128,128]{1,0:T(8,128)(2,1)S(1)}, bf16[128,128]{1,0:T(8,128)(2,1)S(1)}, u32[]{:S(2)}, u32[]{:S(2)}) %collective-permute-start.3) | collective-permute-done | bytes 32800 | tf_op jit(solution)/shard_map/ppermute | solution.py:18
  29.5 1.3 %collective-permute-start.16 = (bf16[128,384]{1,0:T(8,128)(2,1)S(1)}, bf16[128,384]{1,0:T(8,128)(2,1)S(1)}, u32[]{:S(2)}, u32[]{:S(2)}) collective-permute-start(bf16[128,384]{1,0:T(8,128)(2,1)S(1)} %select_convert_fusion.6), channel_id=1, source_target_pairs={{0,2},{2,0},{4,6},{6,4},{8,10},{10,8},{12,14},{14,12},{1,3},{3,1},... | collective-permute-start | bytes 294920 | tf_op jit(solution)/shard_map/ppermute | solution.py:18
  30.9 1.4 %collective-permute-start.11 = (bf16[128,384]{1,0:T(8,128)(2,1)S(1)}, bf16[128,384]{1,0:T(8,128)(2,1)S(1)}, u32[]{:S(2)}, u32[]{:S(2)}) collective-permute-start(bf16[128,384]{1,0:T(8,128)(2,1)S(1)} %select_convert_fusion.7), channel_id=1, source_target_pairs={{0,4},{2,6},{4,0},{6,2},{8,12},{10,14},{12,8},{14,10},{1,5},{3,7},... | collective-permute-start | bytes 294920 | tf_op jit(solution)/shard_map/ppermute | solution.py:18
  32.9 1.3 %collective-permute-done.16 = bf16[128,384]{1,0:T(8,128)(2,1)S(1)} collective-permute-done((bf16[128,384]{1,0:T(8,128)(2,1)S(1)}, bf16[128,384]{1,0:T(8,128)(2,1)S(1)}, u32[]{:S(2)}, u32[]{:S(2)}) %collective-permute-start.16) | collective-permute-done | bytes 98336 | tf_op jit(solution)/shard_map/ppermute | solution.py:18
  34.2 1.4 %collective-permute-start.17 = (bf16[128,384]{1,0:T(8,128)(2,1)S(1)}, bf16[128,384]{1,0:T(8,128)(2,1)S(1)}, u32[]{:S(2)}, u32[]{:S(2)}) collective-permute-start(bf16[128,384]{1,0:T(8,128)(2,1)S(1)} %fusion.39), channel_id=1, source_target_pairs={{0,8},{2,10},{4,12},{6,14},{8,0},{10,2},{12,4},{14,6},{1,9},{3,11}... | collective-permute-start | bytes 294920 | tf_op jit(solution)/shard_map/ppermute | solution.py:18
  35.6 1.0 %collective-permute-done.11 = bf16[128,384]{1,0:T(8,128)(2,1)S(1)} collective-permute-done((bf16[128,384]{1,0:T(8,128)(2,1)S(1)}, bf16[128,384]{1,0:T(8,128)(2,1)S(1)}, u32[]{:S(2)}, u32[]{:S(2)}) %collective-permute-start.11) | collective-permute-done | bytes 98336 | tf_op jit(solution)/shard_map/ppermute | solution.py:18
  36.6 1.1 %collective-permute-start.12 = (bf16[128,384]{1,0:T(8,128)(2,1)S(1)}, bf16[128,384]{1,0:T(8,128)(2,1)S(1)}, u32[]{:S(2)}, u32[]{:S(2)}) collective-permute-start(bf16[128,384]{1,0:T(8,128)(2,1)S(1)} %fusion.38), channel_id=1, source_target_pairs={{0,8},{2,10},{4,12},{6,14},{8,0},{10,2},{12,4},{14,6},{1,9},{3,11}... | collective-permute-start | bytes 294920 | tf_op jit(solution)/shard_map/ppermute | solution.py:18
  37.7 3.3 %collective-permute-done.17 = bf16[128,384]{1,0:T(8,128)(2,1)S(1)} collective-permute-done((bf16[128,384]{1,0:T(8,128)(2,1)S(1)}, bf16[128,384]{1,0:T(8,128)(2,1)S(1)}, u32[]{:S(2)}, u32[]{:S(2)}) %collective-permute-start.17) | collective-permute-done | bytes 98336 | tf_op jit(solution)/shard_map/ppermute | solution.py:18
  41.0 1.2 %collective-permute-start.18 = (bf16[128,384]{1,0:T(8,128)(2,1)S(1)}, bf16[128,384]{1,0:T(8,128)(2,1)S(1)}, u32[]{:S(2)}, u32[]{:S(2)}) collective-permute-start(bf16[128,384]{1,0:T(8,128)(2,1)S(1)} %multiply_convert_fusion), channel_id=1, source_target_pairs={{0,2},{2,0},{4,6},{6,4},{8,10},{10,8},{12,14},{14,12},{1,3},{3,1},... | collective-permute-start | bytes 294920 | tf_op jit(solution)/shard_map/ppermute | solution.py:18
  42.9 1.5 %collective-permute-start.13 = (bf16[128,384]{1,0:T(8,128)(2,1)S(1)}, bf16[128,384]{1,0:T(8,128)(2,1)S(1)}, u32[]{:S(2)}, u32[]{:S(2)}) collective-permute-start(bf16[128,384]{1,0:T(8,128)(2,1)S(1)} %multiply_convert_fusion.1), channel_id=1, source_target_pairs={{0,4},{2,6},{4,0},{6,2},{8,12},{10,14},{12,8},{14,10},{1,5},{3,7},... | collective-permute-start | bytes 294920 | tf_op jit(solution)/shard_map/ppermute | solution.py:18
  44.4 1.3 %collective-permute-done.18 = bf16[128,384]{1,0:T(8,128)(2,1)S(1)} collective-permute-done((bf16[128,384]{1,0:T(8,128)(2,1)S(1)}, bf16[128,384]{1,0:T(8,128)(2,1)S(1)}, u32[]{:S(2)}, u32[]{:S(2)}) %collective-permute-start.18) | collective-permute-done | bytes 98336 | tf_op jit(solution)/shard_map/ppermute | solution.py:18
  45.8 1.1 %collective-permute-start.19 = (bf16[128,768]{1,0:T(8,128)(2,1)S(1)}, bf16[128,768]{1,0:T(8,128)(2,1)S(1)}, u32[]{:S(2)}, u32[]{:S(2)}) collective-permute-start(bf16[128,768]{1,0:T(8,128)(2,1)S(1)} %pad_maximum_fusion.2), channel_id=1, source_target_pairs={{0,4},{2,6},{4,0},{6,2},{8,12},{10,14},{12,8},{14,10},{1,5},{3,7},... | collective-permute-start | bytes 589832 | tf_op jit(solution)/shard_map/ppermute | solution.py:18
  47.6 1.4 %collective-permute-start.14 = (bf16[128,768]{1,0:T(8,128)(2,1)S(1)}, bf16[128,768]{1,0:T(8,128)(2,1)S(1)}, u32[]{:S(2)}, u32[]{:S(2)}) collective-permute-start(bf16[128,768]{1,0:T(8,128)(2,1)S(1)} %pad_maximum_fusion.1), channel_id=1, source_target_pairs={{0,2},{2,0},{4,6},{6,4},{8,10},{10,8},{12,14},{14,12},{1,3},{3,1},... | collective-permute-start | bytes 589832 | tf_op jit(solution)/shard_map/ppermute | solution.py:18
  49.0 2.5 %collective-permute-done.19 = bf16[128,768]{1,0:T(8,128)(2,1)S(1)} collective-permute-done((bf16[128,768]{1,0:T(8,128)(2,1)S(1)}, bf16[128,768]{1,0:T(8,128)(2,1)S(1)}, u32[]{:S(2)}, u32[]{:S(2)}) %collective-permute-start.19) | collective-permute-done | bytes 196640 | tf_op jit(solution)/shard_map/ppermute | solution.py:18
  52.1 1.2 %collective-permute-done.14 = bf16[128,768]{1,0:T(8,128)(2,1)S(1)} collective-permute-done((bf16[128,768]{1,0:T(8,128)(2,1)S(1)}, bf16[128,768]{1,0:T(8,128)(2,1)S(1)}, u32[]{:S(2)}, u32[]{:S(2)}) %collective-permute-start.14) | collective-permute-done | bytes 196640 | tf_op jit(solution)/shard_map/ppermute | solution.py:18
  54.4 1.5 %collective-permute-done.20.other_ref = f32[512,128]{1,0:T(8,128)S(1)} collective-permute-done((f32[512,128]{1,0:T(8,128)S(1)}, f32[512,128]{1,0:T(8,128)S(1)}, u32[]{:S(2)}, u32[]{:S(2)}) %collective-permute-start.20) | collective-permute-done | bytes 262176 | tf_op jit(solution)/shard_map/ppermute | solution.py:18
  56.4 1.7 %collective-permute-start.24 = (f32[72,128]{1,0:T(8,128)S(1)}, f32[72,128]{1,0:T(8,128)S(1)}, u32[]{:S(2)}, u32[]{:S(2)}) collective-permute-start(f32[72,128]{1,0:T(8,128)S(1)} %make_gram.1), channel_id=1, source_target_pairs={{0,10},{1,15},{2,8},{3,13},{4,14},{5,11},{6,12},{7,9},{8,2},{9,7},... | collective-permute-start | bytes 110600 | tf_op jit(solution)/shard_map/ppermute | solution.py:36
  58.1 2.1 %collective-permute-start.23 = (f32[72,128]{1,0:T(8,128)S(1)}, f32[72,128]{1,0:T(8,128)S(1)}, u32[]{:S(2)}, u32[]{:S(2)}) collective-permute-start(f32[72,128]{1,0:T(8,128)S(1)} %make_gram.1), channel_id=1, source_target_pairs={{0,8},{1,13},{2,10},{3,15},{4,12},{5,9},{6,14},{7,11},{8,0},{9,5},... | collective-permute-start | bytes 110600 | tf_op jit(solution)/shard_map/ppermute | solution.py:36
  61.5 1.1 %collective-permute-done.24 = f32[72,128]{1,0:T(8,128)S(1)} collective-permute-done((f32[72,128]{1,0:T(8,128)S(1)}, f32[72,128]{1,0:T(8,128)S(1)}, u32[]{:S(2)}, u32[]{:S(2)}) %collective-permute-start.24) | collective-permute-done | bytes 36896 | tf_op jit(solution)/shard_map/ppermute | solution.py:36
  62.6 1.6 %collective-permute-done.23 = f32[72,128]{1,0:T(8,128)S(1)} collective-permute-done((f32[72,128]{1,0:T(8,128)S(1)}, f32[72,128]{1,0:T(8,128)S(1)}, u32[]{:S(2)}, u32[]{:S(2)}) %collective-permute-start.23) | collective-permute-done | bytes 36896 | tf_op jit(solution)/shard_map/ppermute | solution.py:36
  64.2 1.3 %collective-permute-start.25 = (f32[72,128]{1,0:T(8,128)S(1)}, f32[72,128]{1,0:T(8,128)S(1)}, u32[]{:S(2)}, u32[]{:S(2)}) collective-permute-start(f32[72,128]{1,0:T(8,128)S(1)} %add_add_fusion), channel_id=1, source_target_pairs={{0,1},{1,0},{2,3},{3,2},{4,5},{5,4},{6,7},{7,6},{8,9},{9,8},{10,11... | collective-permute-start | bytes 110600 | tf_op jit(solution)/shard_map/ppermute | solution.py:18
  66.4 4.6 %make_basis.1 = (f32[512,128]{1,0:T(8,128)}, f32[128,512]{1,0:T(8,128)S(1)}, f32[128,512]{1,0:T(8,128)S(1)}, f32[128,1536]{1,0:T(8,128)S(1)}, f32[128,1536]{1,0:T(8,128)S(1)}) custom-call(f32[72,128]{1,0:T(8,128)S(1)} %add.116.gram_ref, f32[512,128]{1,0:T(8,128)S(1)} %fusion.6.mine_ref, f32[512,128]{1,0:T(8,128)S(1)} %collective-permute-done.20.other_ref, ...), custom_call_target="tpu_custom_call" | custom-call | tf_op jit(solution)/shard_map/make_basis/pallas_call | solution.py:294
  71.1 1.4 %collective-permute-start.26 = (bf16[2,2,16,512]{3,2,0,1:T(8,128)(2,1)S(1)}, bf16[2,2,16,512]{3,2,0,1:T(8,128)(2,1)S(1)}, u32[]{:S(2)}, u32[]{:S(2)}) collective-permute-start(bf16[2,2,16,512]{3,2,0,1:T(8,128)(2,1)S(1)} %fusion.28), channel_id=1, source_target_pairs={{0,2},{2,0},{4,6},{6,4},{8,10},{10,8},{12,14},{14,12},{1,3},{3,1},... | collective-permute-start | bytes 196616 | tf_op jit(solution)/shard_map/ppermute | solution.py:18
  72.6 1.8 %collective-permute-start.29 = (bf16[2,2,16,512]{3,2,0,1:T(8,128)(2,1)S(1)}, bf16[2,2,16,512]{3,2,0,1:T(8,128)(2,1)S(1)}, u32[]{:S(2)}, u32[]{:S(2)}) collective-permute-start(bf16[2,2,16,512]{3,2,0,1:T(8,128)(2,1)S(1)} %fusion.29), channel_id=1, source_target_pairs={{0,4},{2,6},{4,0},{6,2},{8,12},{10,14},{12,8},{14,10},{1,5},{3,7},... | collective-permute-start | bytes 196616 | tf_op jit(solution)/shard_map/ppermute | solution.py:18
  75.8 1.8 %collective-permute-start.27 = (bf16[2,16,512]{2,1,0:T(8,128)(2,1)S(1)}, bf16[2,16,512]{2,1,0:T(8,128)(2,1)S(1)}, u32[]{:S(2)}, u32[]{:S(2)}) collective-permute-start(bf16[2,16,512]{2,1,0:T(8,128)(2,1)S(1)} %fusion.32), channel_id=1, source_target_pairs={{0,4},{2,6},{4,0},{6,2},{8,12},{10,14},{12,8},{14,10},{1,5},{3,7},... | collective-permute-start | bytes 98312 | tf_op jit(solution)/shard_map/ppermute | solution.py:18
  77.6 1.8 %collective-permute-start.30 = (bf16[2,16,512]{2,1,0:T(8,128)(2,1)S(1)}, bf16[2,16,512]{2,1,0:T(8,128)(2,1)S(1)}, u32[]{:S(2)}, u32[]{:S(2)}) collective-permute-start(bf16[2,16,512]{2,1,0:T(8,128)(2,1)S(1)} %fusion.33), channel_id=1, source_target_pairs={{0,2},{2,0},{4,6},{6,4},{8,10},{10,8},{12,14},{14,12},{1,3},{3,1},... | collective-permute-start | bytes 98312 | tf_op jit(solution)/shard_map/ppermute | solution.py:18
  79.4 3.0 %collective-permute-done.27 = bf16[2,16,512]{2,1,0:T(8,128)(2,1)S(1)} collective-permute-done((bf16[2,16,512]{2,1,0:T(8,128)(2,1)S(1)}, bf16[2,16,512]{2,1,0:T(8,128)(2,1)S(1)}, u32[]{:S(2)}, u32[]{:S(2)}) %collective-permute-start.27) | collective-permute-done | bytes 32800 | tf_op jit(solution)/shard_map/ppermute | solution.py:18
  82.5 1.3 %collective-permute-start.28 = (bf16[16,512]{1,0:T(8,128)(2,1)S(1)}, bf16[16,512]{1,0:T(8,128)(2,1)S(1)}, u32[]{:S(2)}, u32[]{:S(2)}) collective-permute-start(bf16[16,512]{1,0:T(8,128)(2,1)S(1)} %fusion.36), channel_id=1, source_target_pairs={{0,8},{2,10},{4,12},{6,14},{8,0},{10,2},{12,4},{14,6},{1,9},{3,11}... | collective-permute-start | bytes 49160 | tf_op jit(solution)/shard_map/ppermute | solution.py:18
  83.8 1.8 %collective-permute-start.31 = (bf16[16,512]{1,0:T(8,128)(2,1)S(1)}, bf16[16,512]{1,0:T(8,128)(2,1)S(1)}, u32[]{:S(2)}, u32[]{:S(2)}) collective-permute-start(bf16[16,512]{1,0:T(8,128)(2,1)S(1)} %fusion.37), channel_id=1, source_target_pairs={{0,8},{2,10},{4,12},{6,14},{8,0},{10,2},{12,4},{14,6},{1,9},{3,11}... | collective-permute-start | bytes 49160 | tf_op jit(solution)/shard_map/ppermute | solution.py:18
  85.6 1.6 %collective-permute-done.28 = bf16[16,512]{1,0:T(8,128)(2,1)S(1)} collective-permute-done((bf16[16,512]{1,0:T(8,128)(2,1)S(1)}, bf16[16,512]{1,0:T(8,128)(2,1)S(1)}, u32[]{:S(2)}, u32[]{:S(2)}) %collective-permute-start.28) | collective-permute-done | bytes 16416 | tf_op jit(solution)/shard_map/ppermute | solution.py:18
  87.2 1.3 %collective-permute-done.31 = bf16[16,512]{1,0:T(8,128)(2,1)S(1)} collective-permute-done((bf16[16,512]{1,0:T(8,128)(2,1)S(1)}, bf16[16,512]{1,0:T(8,128)(2,1)S(1)}, u32[]{:S(2)}, u32[]{:S(2)}) %collective-permute-start.31) | collective-permute-done | bytes 16416 | tf_op jit(solution)/shard_map/ppermute | solution.py:18
  88.6 1.9 %collective-permute-start.33 = (bf16[2,16,1536]{2,1,0:T(8,128)(2,1)S(1)}, bf16[2,16,1536]{2,1,0:T(8,128)(2,1)S(1)}, u32[]{:S(2)}, u32[]{:S(2)}) collective-permute-start(bf16[2,16,1536]{2,1,0:T(8,128)(2,1)S(1)} %fusion.24), channel_id=1, source_target_pairs={{0,4},{2,6},{4,0},{6,2},{8,12},{10,14},{12,8},{14,10},{1,5},{3,7},... | collective-permute-start | bytes 294920 | tf_op jit(solution)/shard_map/ppermute | solution.py:18
  90.9 2.9 %collective-permute-done.33 = bf16[2,16,1536]{2,1,0:T(8,128)(2,1)S(1)} collective-permute-done((bf16[2,16,1536]{2,1,0:T(8,128)(2,1)S(1)}, bf16[2,16,1536]{2,1,0:T(8,128)(2,1)S(1)}, u32[]{:S(2)}, u32[]{:S(2)}) %collective-permute-start.33) | collective-permute-done | bytes 98336 | tf_op jit(solution)/shard_map/ppermute | solution.py:18
  93.9 1.6 %collective-permute-start.34 = (bf16[16,1536]{1,0:T(8,128)(2,1)S(1)}, bf16[16,1536]{1,0:T(8,128)(2,1)S(1)}, u32[]{:S(2)}, u32[]{:S(2)}) collective-permute-start(bf16[16,1536]{1,0:T(8,128)(2,1)S(1)} %fusion.30), channel_id=1, source_target_pairs={{0,8},{2,10},{4,12},{6,14},{8,0},{10,2},{12,4},{14,6},{1,9},{3,11}... | collective-permute-start | bytes 147464 | tf_op jit(solution)/shard_map/ppermute | solution.py:18
  95.6 1.4 %collective-permute-start.37 = (bf16[16,1536]{1,0:T(8,128)(2,1)S(1)}, bf16[16,1536]{1,0:T(8,128)(2,1)S(1)}, u32[]{:S(2)}, u32[]{:S(2)}) collective-permute-start(bf16[16,1536]{1,0:T(8,128)(2,1)S(1)} %fusion.31), channel_id=1, source_target_pairs={{0,8},{2,10},{4,12},{6,14},{8,0},{10,2},{12,4},{14,6},{1,9},{3,11}... | collective-permute-start | bytes 147464 | tf_op jit(solution)/shard_map/ppermute | solution.py:18
  97.0 1.9 %collective-permute-done.34 = bf16[16,1536]{1,0:T(8,128)(2,1)S(1)} collective-permute-done((bf16[16,1536]{1,0:T(8,128)(2,1)S(1)}, bf16[16,1536]{1,0:T(8,128)(2,1)S(1)}, u32[]{:S(2)}, u32[]{:S(2)}) %collective-permute-start.34) | collective-permute-done | bytes 49184 | tf_op jit(solution)/shard_map/ppermute | solution.py:18
  98.9 2.2 %collective-permute-done.37 = bf16[16,1536]{1,0:T(8,128)(2,1)S(1)} collective-permute-done((bf16[16,1536]{1,0:T(8,128)(2,1)S(1)}, bf16[16,1536]{1,0:T(8,128)(2,1)S(1)}, u32[]{:S(2)}, u32[]{:S(2)}) %collective-permute-start.37) | collective-permute-done | bytes 49184 | tf_op jit(solution)/shard_map/ppermute | solution.py:18
  (102 shorter events, 13.9 us)
Async XLA Ops:
  0.6 0.9 copy-start
  4.6 5.5 %collective-permute-start.5 = (bf16[128,256]{1,0:T(8,128)(2,1)S(1)}, bf16[128,256]{1,0:T(8,128)(2,1)S(1)}, u32[]{:S(2)}, u32[]{:S(2)}) collective-permute-start(bf16[128,256]{1,0:T(8,128)(2,1)S(1)} %select_convert_fusion.10), channel_id=1, source_target_pairs={{0,4},{2,6},{4,0},{6,2},{8,12},{10,14},{12,8},{14,10},{1,5},{3,7},... | collective-permute-start | bytes 196616 | tf_op jit(solution)/shard_map/ppermute | solution.py:18
  7.7 24.6 %copy-start.1 = (bf16[512,4096]{1,0:T(8,128)(2,1)S(1)}, bf16[512,4096]{1,0:T(8,128)(2,1)}, u32[]{:S(2)}) copy-start(bf16[512,4096]{1,0:T(8,128)(2,1)} %slab_ref.3) | copy-start | bytes 12582916
  7.7 4.9 %collective-permute-start = (bf16[128,256]{1,0:T(8,128)(2,1)S(1)}, bf16[128,256]{1,0:T(8,128)(2,1)S(1)}, u32[]{:S(2)}, u32[]{:S(2)}) collective-permute-start(bf16[128,256]{1,0:T(8,128)(2,1)S(1)} %select_convert_fusion.11), channel_id=1, source_target_pairs={{0,2},{2,0},{4,6},{6,4},{8,10},{10,8},{12,14},{14,12},{1,3},{3,1},... | collective-permute-start | bytes 196616 | tf_op jit(solution)/shard_map/ppermute | solution.py:18
  9.3 20.1 %collective-permute-start.15 = (bf16[128,768]{1,0:T(8,128)(2,1)S(1)}, bf16[128,768]{1,0:T(8,128)(2,1)S(1)}, u32[]{:S(2)}, u32[]{:S(2)}) collective-permute-start(bf16[128,768]{1,0:T(8,128)(2,1)S(1)} %select_convert_fusion.2), channel_id=1, source_target_pairs={{0,4},{2,6},{4,0},{6,2},{8,12},{10,14},{12,8},{14,10},{1,5},{3,7},... | collective-permute-start | bytes 589832 | tf_op jit(solution)/shard_map/ppermute | solution.py:18
  9.8 21.0 %collective-permute-start.10 = (bf16[128,768]{1,0:T(8,128)(2,1)S(1)}, bf16[128,768]{1,0:T(8,128)(2,1)S(1)}, u32[]{:S(2)}, u32[]{:S(2)}) collective-permute-start(bf16[128,768]{1,0:T(8,128)(2,1)S(1)} %select_convert_fusion.3), channel_id=1, source_target_pairs={{0,2},{2,0},{4,6},{6,4},{8,10},{10,8},{12,14},{14,12},{1,3},{3,1},... | collective-permute-start | bytes 589832 | tf_op jit(solution)/shard_map/ppermute | solution.py:18
  10.1 6.9 %collective-permute-start.6 = (bf16[128,128]{1,0:T(8,128)(2,1)S(1)}, bf16[128,128]{1,0:T(8,128)(2,1)S(1)}, u32[]{:S(2)}, u32[]{:S(2)}) collective-permute-start(bf16[128,128]{1,0:T(8,128)(2,1)S(1)} %select_convert_fusion.16), channel_id=1, source_target_pairs={{0,2},{2,0},{4,6},{6,4},{8,10},{10,8},{12,14},{14,12},{1,3},{3,1},... | collective-permute-start | bytes 98312 | tf_op jit(solution)/shard_map/ppermute | solution.py:18
  12.6 7.0 %collective-permute-start.1 = (bf16[128,128]{1,0:T(8,128)(2,1)S(1)}, bf16[128,128]{1,0:T(8,128)(2,1)S(1)}, u32[]{:S(2)}, u32[]{:S(2)}) collective-permute-start(bf16[128,128]{1,0:T(8,128)(2,1)S(1)} %select_convert_fusion.17), channel_id=1, source_target_pairs={{0,4},{2,6},{4,0},{6,2},{8,12},{10,14},{12,8},{14,10},{1,5},{3,7},... | collective-permute-start | bytes 98312 | tf_op jit(solution)/shard_map/ppermute | solution.py:18
  16.9 5.9 %collective-permute-start.7 = (bf16[128,128]{1,0:T(8,128)(2,1)S(1)}, bf16[128,128]{1,0:T(8,128)(2,1)S(1)}, u32[]{:S(2)}, u32[]{:S(2)}) collective-permute-start(bf16[128,128]{1,0:T(8,128)(2,1)S(1)} %fusion.41), channel_id=1, source_target_pairs={{0,8},{2,10},{4,12},{6,14},{8,0},{10,2},{12,4},{14,6},{1,9},{3,11}... | collective-permute-start | bytes 98312 | tf_op jit(solution)/shard_map/ppermute | solution.py:18
  19.6 4.9 %collective-permute-start.2 = (bf16[128,128]{1,0:T(8,128)(2,1)S(1)}, bf16[128,128]{1,0:T(8,128)(2,1)S(1)}, u32[]{:S(2)}, u32[]{:S(2)}) collective-permute-start(bf16[128,128]{1,0:T(8,128)(2,1)S(1)} %fusion.40), channel_id=1, source_target_pairs={{0,8},{2,10},{4,12},{6,14},{8,0},{10,2},{12,4},{14,6},{1,9},{3,11}... | collective-permute-start | bytes 98312 | tf_op jit(solution)/shard_map/ppermute | solution.py:18
  22.9 4.0 %collective-permute-start.8 = (bf16[128,128]{1,0:T(8,128)(2,1)S(1)}, bf16[128,128]{1,0:T(8,128)(2,1)S(1)}, u32[]{:S(2)}, u32[]{:S(2)}) collective-permute-start(bf16[128,128]{1,0:T(8,128)(2,1)S(1)} %multiply_convert_fusion.2), channel_id=1, source_target_pairs={{0,2},{2,0},{4,6},{6,4},{8,10},{10,8},{12,14},{14,12},{1,3},{3,1},... | collective-permute-start | bytes 98312 | tf_op jit(solution)/shard_map/ppermute | solution.py:18
  24.5 4.0 %collective-permute-start.3 = (bf16[128,128]{1,0:T(8,128)(2,1)S(1)}, bf16[128,128]{1,0:T(8,128)(2,1)S(1)}, u32[]{:S(2)}, u32[]{:S(2)}) collective-permute-start(bf16[128,128]{1,0:T(8,128)(2,1)S(1)} %multiply_convert_fusion.3), channel_id=1, source_target_pairs={{0,4},{2,6},{4,0},{6,2},{8,12},{10,14},{12,8},{14,10},{1,5},{3,7},... | collective-permute-start | bytes 98312 | tf_op jit(solution)/shard_map/ppermute | solution.py:18
  26.9 5.4 %collective-permute-start.9 = (bf16[128,256]{1,0:T(8,128)(2,1)S(1)}, bf16[128,256]{1,0:T(8,128)(2,1)S(1)}, u32[]{:S(2)}, u32[]{:S(2)}) collective-permute-start(bf16[128,256]{1,0:T(8,128)(2,1)S(1)} %pad_maximum_fusion.4), channel_id=1, source_target_pairs={{0,4},{2,6},{4,0},{6,2},{8,12},{10,14},{12,8},{14,10},{1,5},{3,7},... | collective-permute-start | bytes 196616 | tf_op jit(solution)/shard_map/ppermute | solution.py:18
  28.5 4.3 %collective-permute-start.4 = (bf16[128,256]{1,0:T(8,128)(2,1)S(1)}, bf16[128,256]{1,0:T(8,128)(2,1)S(1)}, u32[]{:S(2)}, u32[]{:S(2)}) collective-permute-start(bf16[128,256]{1,0:T(8,128)(2,1)S(1)} %pad_maximum_fusion.3), channel_id=1, source_target_pairs={{0,2},{2,0},{4,6},{6,4},{8,10},{10,8},{12,14},{14,12},{1,3},{3,1},... | collective-permute-start | bytes 196616 | tf_op jit(solution)/shard_map/ppermute | solution.py:18
  29.5 4.7 %collective-permute-start.16 = (bf16[128,384]{1,0:T(8,128)(2,1)S(1)}, bf16[128,384]{1,0:T(8,128)(2,1)S(1)}, u32[]{:S(2)}, u32[]{:S(2)}) collective-permute-start(bf16[128,384]{1,0:T(8,128)(2,1)S(1)} %select_convert_fusion.6), channel_id=1, source_target_pairs={{0,2},{2,0},{4,6},{6,4},{8,10},{10,8},{12,14},{14,12},{1,3},{3,1},... | collective-permute-start | bytes 294920 | tf_op jit(solution)/shard_map/ppermute | solution.py:18
  30.9 5.7 %collective-permute-start.11 = (bf16[128,384]{1,0:T(8,128)(2,1)S(1)}, bf16[128,384]{1,0:T(8,128)(2,1)S(1)}, u32[]{:S(2)}, u32[]{:S(2)}) collective-permute-start(bf16[128,384]{1,0:T(8,128)(2,1)S(1)} %select_convert_fusion.7), channel_id=1, source_target_pairs={{0,4},{2,6},{4,0},{6,2},{8,12},{10,14},{12,8},{14,10},{1,5},{3,7},... | collective-permute-start | bytes 294920 | tf_op jit(solution)/shard_map/ppermute | solution.py:18
  34.2 6.7 %collective-permute-start.17 = (bf16[128,384]{1,0:T(8,128)(2,1)S(1)}, bf16[128,384]{1,0:T(8,128)(2,1)S(1)}, u32[]{:S(2)}, u32[]{:S(2)}) collective-permute-start(bf16[128,384]{1,0:T(8,128)(2,1)S(1)} %fusion.39), channel_id=1, source_target_pairs={{0,8},{2,10},{4,12},{6,14},{8,0},{10,2},{12,4},{14,6},{1,9},{3,11}... | collective-permute-start | bytes 294920 | tf_op jit(solution)/shard_map/ppermute | solution.py:18
  36.6 6.2 %collective-permute-start.12 = (bf16[128,384]{1,0:T(8,128)(2,1)S(1)}, bf16[128,384]{1,0:T(8,128)(2,1)S(1)}, u32[]{:S(2)}, u32[]{:S(2)}) collective-permute-start(bf16[128,384]{1,0:T(8,128)(2,1)S(1)} %fusion.38), channel_id=1, source_target_pairs={{0,8},{2,10},{4,12},{6,14},{8,0},{10,2},{12,4},{14,6},{1,9},{3,11}... | collective-permute-start | bytes 294920 | tf_op jit(solution)/shard_map/ppermute | solution.py:18
  41.0 4.7 %collective-permute-start.18 = (bf16[128,384]{1,0:T(8,128)(2,1)S(1)}, bf16[128,384]{1,0:T(8,128)(2,1)S(1)}, u32[]{:S(2)}, u32[]{:S(2)}) collective-permute-start(bf16[128,384]{1,0:T(8,128)(2,1)S(1)} %multiply_convert_fusion), channel_id=1, source_target_pairs={{0,2},{2,0},{4,6},{6,4},{8,10},{10,8},{12,14},{14,12},{1,3},{3,1},... | collective-permute-start | bytes 294920 | tf_op jit(solution)/shard_map/ppermute | solution.py:18
  42.9 4.7 %collective-permute-start.13 = (bf16[128,384]{1,0:T(8,128)(2,1)S(1)}, bf16[128,384]{1,0:T(8,128)(2,1)S(1)}, u32[]{:S(2)}, u32[]{:S(2)}) collective-permute-start(bf16[128,384]{1,0:T(8,128)(2,1)S(1)} %multiply_convert_fusion.1), channel_id=1, source_target_pairs={{0,4},{2,6},{4,0},{6,2},{8,12},{10,14},{12,8},{14,10},{1,5},{3,7},... | collective-permute-start | bytes 294920 | tf_op jit(solution)/shard_map/ppermute | solution.py:18
  45.8 5.7 %collective-permute-start.19 = (bf16[128,768]{1,0:T(8,128)(2,1)S(1)}, bf16[128,768]{1,0:T(8,128)(2,1)S(1)}, u32[]{:S(2)}, u32[]{:S(2)}) collective-permute-start(bf16[128,768]{1,0:T(8,128)(2,1)S(1)} %pad_maximum_fusion.2), channel_id=1, source_target_pairs={{0,4},{2,6},{4,0},{6,2},{8,12},{10,14},{12,8},{14,10},{1,5},{3,7},... | collective-permute-start | bytes 589832 | tf_op jit(solution)/shard_map/ppermute | solution.py:18
  47.6 5.7 %collective-permute-start.14 = (bf16[128,768]{1,0:T(8,128)(2,1)S(1)}, bf16[128,768]{1,0:T(8,128)(2,1)S(1)}, u32[]{:S(2)}, u32[]{:S(2)}) collective-permute-start(bf16[128,768]{1,0:T(8,128)(2,1)S(1)} %pad_maximum_fusion.1), channel_id=1, source_target_pairs={{0,2},{2,0},{4,6},{6,4},{8,10},{10,8},{12,14},{14,12},{1,3},{3,1},... | collective-permute-start | bytes 589832 | tf_op jit(solution)/shard_map/ppermute | solution.py:18
  54.3 1.6 %collective-permute-start.20 = (f32[512,128]{1,0:T(8,128)S(1)}, f32[512,128]{1,0:T(8,128)S(1)}, u32[]{:S(2)}, u32[]{:S(2)}) collective-permute-start(f32[512,128]{1,0:T(8,128)S(1)} %fusion.6.mine_ref), channel_id=1, source_target_pairs={{0,1},{1,0},{2,3},{3,2},{4,5},{5,4},{6,7},{7,6},{8,9},{9,8},{10,11... | collective-permute-start | bytes 786440 | tf_op jit(solution)/shard_map/ppermute | solution.py:18
  56.4 6.2 %collective-permute-start.24 = (f32[72,128]{1,0:T(8,128)S(1)}, f32[72,128]{1,0:T(8,128)S(1)}, u32[]{:S(2)}, u32[]{:S(2)}) collective-permute-start(f32[72,128]{1,0:T(8,128)S(1)} %make_gram.1), channel_id=1, source_target_pairs={{0,10},{1,15},{2,8},{3,13},{4,14},{5,11},{6,12},{7,9},{8,2},{9,7},... | collective-permute-start | bytes 110600 | tf_op jit(solution)/shard_map/ppermute | solution.py:36
  58.1 6.1 %collective-permute-start.23 = (f32[72,128]{1,0:T(8,128)S(1)}, f32[72,128]{1,0:T(8,128)S(1)}, u32[]{:S(2)}, u32[]{:S(2)}) collective-permute-start(f32[72,128]{1,0:T(8,128)S(1)} %make_gram.1), channel_id=1, source_target_pairs={{0,8},{1,13},{2,10},{3,15},{4,12},{5,9},{6,14},{7,11},{8,0},{9,5},... | collective-permute-start | bytes 110600 | tf_op jit(solution)/shard_map/ppermute | solution.py:36
  60.2 4.0 %collective-permute-start.22 = (f32[72,128]{1,0:T(8,128)S(1)}, f32[72,128]{1,0:T(8,128)S(1)}, u32[]{:S(2)}, u32[]{:S(2)}) collective-permute-start(f32[72,128]{1,0:T(8,128)S(1)} %make_gram.1), channel_id=1, source_target_pairs={{0,2},{1,7},{2,0},{3,5},{4,6},{5,3},{6,4},{7,1},{8,10},{9,15},{10,... | collective-permute-start | bytes 110600 | tf_op jit(solution)/shard_map/ppermute | solution.py:36
  60.8 3.3 %collective-permute-start.21 = (f32[72,128]{1,0:T(8,128)S(1)}, f32[72,128]{1,0:T(8,128)S(1)}, u32[]{:S(2)}, u32[]{:S(2)}) collective-permute-start(f32[72,128]{1,0:T(8,128)S(1)} %make_gram.1), channel_id=1, source_target_pairs={{1,5},{3,7},{5,1},{7,3},{9,13},{11,15},{13,9},{15,11},{17,21},{19,... | collective-permute-start | bytes 110600 | tf_op jit(solution)/shard_map/ppermute | solution.py:36
  64.2 2.2 %collective-permute-start.25 = (f32[72,128]{1,0:T(8,128)S(1)}, f32[72,128]{1,0:T(8,128)S(1)}, u32[]{:S(2)}, u32[]{:S(2)}) collective-permute-start(f32[72,128]{1,0:T(8,128)S(1)} %add_add_fusion), channel_id=1, source_target_pairs={{0,1},{1,0},{2,3},{3,2},{4,5},{5,4},{6,7},{7,6},{8,9},{9,8},{10,11... | collective-permute-start | bytes 110600 | tf_op jit(solution)/shard_map/ppermute | solution.py:18
  71.1 4.6 %collective-permute-start.26 = (bf16[2,2,16,512]{3,2,0,1:T(8,128)(2,1)S(1)}, bf16[2,2,16,512]{3,2,0,1:T(8,128)(2,1)S(1)}, u32[]{:S(2)}, u32[]{:S(2)}) collective-permute-start(bf16[2,2,16,512]{3,2,0,1:T(8,128)(2,1)S(1)} %fusion.28), channel_id=1, source_target_pairs={{0,2},{2,0},{4,6},{6,4},{8,10},{10,8},{12,14},{14,12},{1,3},{3,1},... | collective-permute-start | bytes 196616 | tf_op jit(solution)/shard_map/ppermute | solution.py:18
  72.6 5.0 %collective-permute-start.29 = (bf16[2,2,16,512]{3,2,0,1:T(8,128)(2,1)S(1)}, bf16[2,2,16,512]{3,2,0,1:T(8,128)(2,1)S(1)}, u32[]{:S(2)}, u32[]{:S(2)}) collective-permute-start(bf16[2,2,16,512]{3,2,0,1:T(8,128)(2,1)S(1)} %fusion.29), channel_id=1, source_target_pairs={{0,4},{2,6},{4,0},{6,2},{8,12},{10,14},{12,8},{14,10},{1,5},{3,7},... | collective-permute-start | bytes 196616 | tf_op jit(solution)/shard_map/ppermute | solution.py:18
  74.5 14.0 %collective-permute-start.32 = (bf16[2,2,16,1536]{3,2,0,1:T(8,128)(2,1)S(1)}, bf16[2,2,16,1536]{3,2,0,1:T(8,128)(2,1)S(1)}, u32[]{:S(2)}, u32[]{:S(2)}) collective-permute-start(bf16[2,2,16,1536]{3,2,0,1:T(8,128)(2,1)S(1)} %fusion.16), channel_id=1, source_target_pairs={{0,2},{2,0},{4,6},{6,4},{8,10},{10,8},{12,14},{14,12},{1,3},{3,1},... | collective-permute-start | bytes 589832 | tf_op jit(solution)/shard_map/ppermute | solution.py:18
  75.3 15.1 %collective-permute-start.35 = (bf16[2,2,16,1536]{3,2,0,1:T(8,128)(2,1)S(1)}, bf16[2,2,16,1536]{3,2,0,1:T(8,128)(2,1)S(1)}, u32[]{:S(2)}, u32[]{:S(2)}) collective-permute-start(bf16[2,2,16,1536]{3,2,0,1:T(8,128)(2,1)S(1)} %fusion.17), channel_id=1, source_target_pairs={{0,4},{2,6},{4,0},{6,2},{8,12},{10,14},{12,8},{14,10},{1,5},{3,7},... | collective-permute-start | bytes 589832 | tf_op jit(solution)/shard_map/ppermute | solution.py:18
  75.8 6.7 %collective-permute-start.27 = (bf16[2,16,512]{2,1,0:T(8,128)(2,1)S(1)}, bf16[2,16,512]{2,1,0:T(8,128)(2,1)S(1)}, u32[]{:S(2)}, u32[]{:S(2)}) collective-permute-start(bf16[2,16,512]{2,1,0:T(8,128)(2,1)S(1)} %fusion.32), channel_id=1, source_target_pairs={{0,4},{2,6},{4,0},{6,2},{8,12},{10,14},{12,8},{14,10},{1,5},{3,7},... | collective-permute-start | bytes 98312 | tf_op jit(solution)/shard_map/ppermute | solution.py:18
  77.6 6.1 %collective-permute-start.30 = (bf16[2,16,512]{2,1,0:T(8,128)(2,1)S(1)}, bf16[2,16,512]{2,1,0:T(8,128)(2,1)S(1)}, u32[]{:S(2)}, u32[]{:S(2)}) collective-permute-start(bf16[2,16,512]{2,1,0:T(8,128)(2,1)S(1)} %fusion.33), channel_id=1, source_target_pairs={{0,2},{2,0},{4,6},{6,4},{8,10},{10,8},{12,14},{14,12},{1,3},{3,1},... | collective-permute-start | bytes 98312 | tf_op jit(solution)/shard_map/ppermute | solution.py:18
  82.5 4.7 %collective-permute-start.28 = (bf16[16,512]{1,0:T(8,128)(2,1)S(1)}, bf16[16,512]{1,0:T(8,128)(2,1)S(1)}, u32[]{:S(2)}, u32[]{:S(2)}) collective-permute-start(bf16[16,512]{1,0:T(8,128)(2,1)S(1)} %fusion.36), channel_id=1, source_target_pairs={{0,8},{2,10},{4,12},{6,14},{8,0},{10,2},{12,4},{14,6},{1,9},{3,11}... | collective-permute-start | bytes 49160 | tf_op jit(solution)/shard_map/ppermute | solution.py:18
  83.8 4.7 %collective-permute-start.31 = (bf16[16,512]{1,0:T(8,128)(2,1)S(1)}, bf16[16,512]{1,0:T(8,128)(2,1)S(1)}, u32[]{:S(2)}, u32[]{:S(2)}) collective-permute-start(bf16[16,512]{1,0:T(8,128)(2,1)S(1)} %fusion.37), channel_id=1, source_target_pairs={{0,8},{2,10},{4,12},{6,14},{8,0},{10,2},{12,4},{14,6},{1,9},{3,11}... | collective-permute-start | bytes 49160 | tf_op jit(solution)/shard_map/ppermute | solution.py:18
  88.6 5.2 %collective-permute-start.33 = (bf16[2,16,1536]{2,1,0:T(8,128)(2,1)S(1)}, bf16[2,16,1536]{2,1,0:T(8,128)(2,1)S(1)}, u32[]{:S(2)}, u32[]{:S(2)}) collective-permute-start(bf16[2,16,1536]{2,1,0:T(8,128)(2,1)S(1)} %fusion.24), channel_id=1, source_target_pairs={{0,4},{2,6},{4,0},{6,2},{8,12},{10,14},{12,8},{14,10},{1,5},{3,7},... | collective-permute-start | bytes 294920 | tf_op jit(solution)/shard_map/ppermute | solution.py:18
  90.6 4.9 %collective-permute-start.36 = (bf16[2,16,1536]{2,1,0:T(8,128)(2,1)S(1)}, bf16[2,16,1536]{2,1,0:T(8,128)(2,1)S(1)}, u32[]{:S(2)}, u32[]{:S(2)}) collective-permute-start(bf16[2,16,1536]{2,1,0:T(8,128)(2,1)S(1)} %fusion.25), channel_id=1, source_target_pairs={{0,2},{2,0},{4,6},{6,4},{8,10},{10,8},{12,14},{14,12},{1,3},{3,1},... | collective-permute-start | bytes 294920 | tf_op jit(solution)/shard_map/ppermute | solution.py:18
  93.9 5.1 %collective-permute-start.34 = (bf16[16,1536]{1,0:T(8,128)(2,1)S(1)}, bf16[16,1536]{1,0:T(8,128)(2,1)S(1)}, u32[]{:S(2)}, u32[]{:S(2)}) collective-permute-start(bf16[16,1536]{1,0:T(8,128)(2,1)S(1)} %fusion.30), channel_id=1, source_target_pairs={{0,8},{2,10},{4,12},{6,14},{8,0},{10,2},{12,4},{14,6},{1,9},{3,11}... | collective-permute-start | bytes 147464 | tf_op jit(solution)/shard_map/ppermute | solution.py:18
  95.6 5.6 %collective-permute-start.37 = (bf16[16,1536]{1,0:T(8,128)(2,1)S(1)}, bf16[16,1536]{1,0:T(8,128)(2,1)S(1)}, u32[]{:S(2)}, u32[]{:S(2)}) collective-permute-start(bf16[16,1536]{1,0:T(8,128)(2,1)S(1)} %fusion.31), channel_id=1, source_target_pairs={{0,8},{2,10},{4,12},{6,14},{8,0},{10,2},{12,4},{14,6},{1,9},{3,11}... | collective-permute-start | bytes 147464 | tf_op jit(solution)/shard_map/ppermute | solution.py:18

commit v19 on v15

--- a/solution.py
+++ b/solution.py
@@ -42,6 +42,31 @@
     return value
 
 
+def bit_of(axis, bit):
+    return lax.rem(lax.div(lax.axis_index(axis), 1 << bit), 2)
+
+
+def pick(upper, low, high):
+    return jnp.where(upper, high, low), jnp.where(upper, low, high).astype(jnp.bfloat16)
+
+
+def sum_and_share(value, axis, order, scale):
+    for bit in order[:-1]:
+        half = value.shape[1] // 2
+        keep, send = pick(bit_of(axis, bit) == 1, value[:, :half], value[:, half:])
+        landed = yield send, bit
+        value = keep + landed.astype(jnp.float32)
+    landed = yield value.astype(jnp.bfloat16), order[-1]
+    block = ((value + landed.astype(jnp.float32)) * scale).astype(jnp.bfloat16)
+    for bit in reversed(order[:-1]):
+        upper = bit_of(axis, bit) == 1
+        other = yield block, bit
+        block = jnp.concatenate(
+            [jnp.where(upper, other, block), jnp.where(upper, block, other)], axis=1
+        )
+    return block
+
+
 def scatter_sum(value, axis, order):
     rows, cols = value.shape[0] >> len(order), value.shape[1]
     total = value.reshape([2] * len(order) + [rows, cols])
@@ -51,34 +76,42 @@
         left.remove(bit)
         low = lax.index_in_dim(total, 0, dim, keepdims=False)
         high = lax.index_in_dim(total, 1, dim, keepdims=False)
-        upper = bit_of(axis, bit) == 1
-        send = jnp.where(upper, low, high).astype(jnp.bfloat16)
-        landed = swap(send, axis, 1 << bit)
-        total = jnp.where(upper, high, low) + landed.astype(jnp.float32)
+        keep, send = pick(bit_of(axis, bit) == 1, low, high)
+        landed = yield send, bit
+        total = keep + landed.astype(jnp.float32)
     return total
 
 
-def bit_of(axis, bit):
-    return lax.rem(lax.div(lax.axis_index(axis), 1 << bit), 2)
-
-
-def sum_and_share(value, axis, order, scale):
-    for bit in order[:-1]:
-        upper = bit_of(axis, bit) == 1
-        half = value.shape[1] // 2
-        low, high = value[:, :half], value[:, half:]
-        send = jnp.where(upper, low, high).astype(jnp.bfloat16)
-        landed = swap(send, axis, 1 << bit)
-        value = jnp.where(upper, high, low) + landed.astype(jnp.float32)
-    landed = swap(value.astype(jnp.bfloat16), axis, 1 << order[-1])
-    block = ((value + landed.astype(jnp.float32)) * scale).astype(jnp.bfloat16)
-    for bit in reversed(order[:-1]):
-        upper = bit_of(axis, bit) == 1
-        other = swap(block, axis, 1 << bit)
-        block = jnp.concatenate(
-            [jnp.where(upper, other, block), jnp.where(upper, block, other)], axis=1
-        )
-    return block
+def after(value, others):
+    return lax.optimization_barrier((value, others))[0] if others else value
+
+
+def staggered(steps, values, axis, *args):
+    orders = orders_of(axis)
+    pairs = [range(c, c + 2) for c in range(0, len(values), 2)]
+    running, landed, results = {}, {}, {}
+    sends, turn = [], 0
+    while len(results) < len(values):
+        for number, pair in enumerate(pairs):
+            if turn < number or pair[0] in results:
+                continue
+            made = []
+            for c in pair:
+                try:
+                    if c in running:
+                        send, bit = running[c].send(after(landed[c], sends))
+                    else:
+                        value = after(values[c], sends)
+                        running[c] = steps(value, axis, orders[c % 2], *args)
+                        send, bit = next(running[c])
+                except StopIteration as end:
+                    results[c] = end.value
+                    continue
+                made.append(send)
+                landed[c] = swap(send, axis, 1 << bit)
+            sends = made or sends
+        turn += 1
+    return [results[c] for c in range(len(values))]
 
 
 def orders_of(axis):
@@ -303,14 +336,13 @@
 
     local_cols = first_product(start_sketch, activations, CHUNKS)
     partial_sketch = 0.0
-    orders = orders_of("row")
     step = cols_here // CHUNKS
-    for c in range(CHUNKS):
+    shared = staggered(sum_and_share, local_cols, "row", 1.0 / root_rows)
+    for c, chunk in enumerate(shared):
         span = slice(c * step, (c + 1) * step)
-        shared = sum_and_share(local_cols[c], "row", orders[c % 2], 1.0 / root_rows)
         partial_sketch = partial_sketch + lax.dot_general(
             activations[:, span],
-            shared,
+            chunk,
             (((1,), (1,)), ((), ())),
             preferred_element_type=jnp.float32,
         )
@@ -320,10 +352,7 @@
         gram, partial_sketch, other_sketch, activations, total_cols, root_rows, CHUNKS
     )
 
-    pieces = [
-        scatter_sum(product, "row", orders[c % 2]) / total_rows
-        for c, product in enumerate(products)
-    ]
+    pieces = [total / total_rows for total in staggered(scatter_sum, products, "row")]
     return (basis, jnp.concatenate(pieces, axis=1))
 
 

time: 82.8 us -> 92.2 us (1.11)
  waiting for transfers between devices: 19.5 us -> 30.3 us
  starting transfers between devices: 49 us -> 47.5 us
    ppermute x34, waiting for transfers between devices: 17 us -> 27.4 us  [swap(): return lax.ppermute(value, axis, [(i, i ^ distance) for i in range(size)])]
    ppermute x34, starting transfers between devices: 43.9 us -> 42.4 us  [swap(): return lax.ppermute(value, axis, [(i, i ^ distance) for i in range(size)])]
  transfers between devices with their start and end apart: 38 -> 38, of which waited for: 18 -> 22; matrix products, arithmetic and copies ran while one was open for 3% -> 3% of each run, Pallas kernels for 0% -> 0%
where the time goes in v19:
time: 92.2 us; the launch traced here: 92 us
  starting transfers between devices  47.5 us (52%)
  waiting for transfers between devices  30.3 us (33%)
  Pallas kernels  8.11 us (9%)
  other arithmetic  2.17 us (2%)
  matrix products  1.78 us (2%)
  between operations  1.12 us (1%)
  local copies, waits for them, and re-layouts  1.05 us (1%)
    ppermute x34, starting transfers between devices, swap(): return lax.ppermute(value, axis, [(i, i ^ distance) for i in range(size)])  42.4 us
    ppermute x34, waiting for transfers between devices, swap(): return lax.ppermute(value, axis, [(i, i ^ distance) for i in range(size)])  27.4 us
    ppermute x4, starting transfers between devices, row_sum(): terms.append(lax.ppermute(value, ('row', 'col'), pairs))  5.1 us
    pallas_call x1, Pallas kernels, make_basis(): pl.pallas_call(functools.partial(basis_kernel, total_cols, root_rows), ou...  4.63 us
    pallas_call x1, Pallas kernels, first_product(): pl.pallas_call(sketch_kernel, out_shape=[jax.ShapeDtypeStruct((width, col...  2.99 us
    ppermute x4, waiting for transfers between devices, row_sum(): terms.append(lax.ppermute(value, ('row', 'col'), pairs))  2.92 us
  transfers between devices with their start and end apart: 38, of which 22 were waited for; matrix products, arithmetic and copies ran while one was open for 3% of the time, Pallas kernels for 0%

profile of v19, /device:TPU:0, one launch (start us, length us, event | category | flops | bytes accessed | tf_op | source)
XLA Modules:
  0.0 92.0 jit_solution(6096346609391780170)
XLA Ops:
  0.7 0.9 copy-done
  1.6 3.0 %first_product.1 = (f32[128,1024]{1,0:T(8,128)S(1)}, f32[128,1024]{1,0:T(8,128)S(1)}, f32[128,1024]{1,0:T(8,128)S(1)}, f32[128,1024]{1,0:T(8,128)S(1)}) custom-call(bf16[512,128]{1,0:T(8,128)(2,1)S(1)} %copy-done, bf16[512,4096]{1,0:T(8,128)(2,1)} %slab_ref.3), custom_call_target="tpu_custom_call" | custom-call | flops 536870912 | bytes 4194304 | tf_op jit(solution)/shard_map/first_product/pallas_call | solution.py:151
  4.6 3.1 %collective-permute-start.2 = (bf16[128,512]{1,0:T(8,128)(2,1)S(1)}, bf16[128,512]{1,0:T(8,128)(2,1)S(1)}, u32[]{:S(2)}, u32[]{:S(2)}) collective-permute-start(bf16[128,512]{1,0:T(8,128)(2,1)S(1)} %select_convert_fusion.6), channel_id=1, source_target_pairs={{0,4},{2,6},{4,0},{6,2},{8,12},{10,14},{12,8},{14,10},{1,5},{3,7},... | collective-permute-start | bytes 393224 | tf_op jit(solution)/shard_map/ppermute | solution.py:18
  7.7 1.6 %collective-permute-start = (bf16[128,512]{1,0:T(8,128)(2,1)S(1)}, bf16[128,512]{1,0:T(8,128)(2,1)S(1)}, u32[]{:S(2)}, u32[]{:S(2)}) collective-permute-start(bf16[128,512]{1,0:T(8,128)(2,1)S(1)} %select_convert_fusion.7), channel_id=1, source_target_pairs={{0,2},{2,0},{4,6},{6,4},{8,10},{10,8},{12,14},{14,12},{1,3},{3,1},... | collective-permute-start | bytes 393224 | tf_op jit(solution)/shard_map/ppermute | solution.py:18
  9.3 1.9 %collective-permute-done.2 = bf16[128,512]{1,0:T(8,128)(2,1)S(1)} collective-permute-done((bf16[128,512]{1,0:T(8,128)(2,1)S(1)}, bf16[128,512]{1,0:T(8,128)(2,1)S(1)}, u32[]{:S(2)}, u32[]{:S(2)}) %collective-permute-start.2) | collective-permute-done | bytes 131104 | tf_op jit(solution)/shard_map/ppermute | solution.py:18
  11.3 1.7 %collective-permute-start.5 = (bf16[128,256]{1,0:T(8,128)(2,1)S(1)}, bf16[128,256]{1,0:T(8,128)(2,1)S(1)}, u32[]{:S(2)}, u32[]{:S(2)}) collective-permute-start(bf16[128,256]{1,0:T(8,128)(2,1)S(1)} %select_convert_fusion.14), channel_id=1, source_target_pairs={{0,2},{2,0},{4,6},{6,4},{8,10},{10,8},{12,14},{14,12},{1,3},{3,1},... | collective-permute-start | bytes 196616 | tf_op jit(solution)/shard_map/ppermute | solution.py:18
  13.1 1.6 %collective-permute-start.1 = (bf16[128,256]{1,0:T(8,128)(2,1)S(1)}, bf16[128,256]{1,0:T(8,128)(2,1)S(1)}, u32[]{:S(2)}, u32[]{:S(2)}) collective-permute-start(bf16[128,256]{1,0:T(8,128)(2,1)S(1)} %select_convert_fusion.15), channel_id=1, source_target_pairs={{0,4},{2,6},{4,0},{6,2},{8,12},{10,14},{12,8},{14,10},{1,5},{3,7},... | collective-permute-start | bytes 196616 | tf_op jit(solution)/shard_map/ppermute | solution.py:18
  15.3 1.3 %collective-permute-start.4 = (bf16[128,512]{1,0:T(8,128)(2,1)S(1)}, bf16[128,512]{1,0:T(8,128)(2,1)S(1)}, u32[]{:S(2)}, u32[]{:S(2)}) collective-permute-start(bf16[128,512]{1,0:T(8,128)(2,1)S(1)} %select_convert_fusion.5), channel_id=1, source_target_pairs={{0,2},{2,0},{4,6},{6,4},{8,10},{10,8},{12,14},{14,12},{1,3},{3,1},... | collective-permute-start | bytes 393224 | tf_op jit(solution)/shard_map/ppermute | solution.py:18
  16.5 1.4 %collective-permute-done.1 = bf16[128,256]{1,0:T(8,128)(2,1)S(1)} collective-permute-done((bf16[128,256]{1,0:T(8,128)(2,1)S(1)}, bf16[128,256]{1,0:T(8,128)(2,1)S(1)}, u32[]{:S(2)}, u32[]{:S(2)}) %collective-permute-start.1) | collective-permute-done | bytes 65568 | tf_op jit(solution)/shard_map/ppermute | solution.py:18
  18.0 2.8 %collective-permute-start.9 = (bf16[128,256]{1,0:T(8,128)(2,1)S(1)}, bf16[128,256]{1,0:T(8,128)(2,1)S(1)}, u32[]{:S(2)}, u32[]{:S(2)}) collective-permute-start(bf16[128,256]{1,0:T(8,128)(2,1)S(1)} %fusion.35), channel_id=1, source_target_pairs={{0,8},{2,10},{4,12},{6,14},{8,0},{10,2},{12,4},{14,6},{1,9},{3,11}... | collective-permute-start | bytes 196616 | tf_op jit(solution)/shard_map/ppermute | solution.py:18
  21.1 1.1 %collective-permute-start.10 = (bf16[128,256]{1,0:T(8,128)(2,1)S(1)}, bf16[128,256]{1,0:T(8,128)(2,1)S(1)}, u32[]{:S(2)}, u32[]{:S(2)}) collective-permute-start(bf16[128,256]{1,0:T(8,128)(2,1)S(1)} %select_convert_fusion.12), channel_id=1, source_target_pairs={{0,2},{2,0},{4,6},{6,4},{8,10},{10,8},{12,14},{14,12},{1,3},{3,1},... | collective-permute-start | bytes 196616 | tf_op jit(solution)/shard_map/ppermute | solution.py:18
  22.3 0.8 collective-permute-start.8
  23.1 1.2 %collective-permute-done.9 = bf16[128,256]{1,0:T(8,128)(2,1)S(1)} collective-permute-done((bf16[128,256]{1,0:T(8,128)(2,1)S(1)}, bf16[128,256]{1,0:T(8,128)(2,1)S(1)}, u32[]{:S(2)}, u32[]{:S(2)}) %collective-permute-start.9) | collective-permute-done | bytes 65568 | tf_op jit(solution)/shard_map/ppermute | solution.py:18
  24.4 2.3 %collective-permute-done.3 = bf16[128,256]{1,0:T(8,128)(2,1)S(1)} collective-permute-done((bf16[128,256]{1,0:T(8,128)(2,1)S(1)}, bf16[128,256]{1,0:T(8,128)(2,1)S(1)}, u32[]{:S(2)}, u32[]{:S(2)}) %collective-permute-start.3) | collective-permute-done | bytes 65568 | tf_op jit(solution)/shard_map/ppermute | solution.py:18
  27.4 1.1 %collective-permute-start.13 = (bf16[128,256]{1,0:T(8,128)(2,1)S(1)}, bf16[128,256]{1,0:T(8,128)(2,1)S(1)}, u32[]{:S(2)}, u32[]{:S(2)}) collective-permute-start(bf16[128,256]{1,0:T(8,128)(2,1)S(1)} %multiply_convert_fusion.2), channel_id=1, source_target_pairs={{0,2},{2,0},{4,6},{6,4},{8,10},{10,8},{12,14},{14,12},{1,3},{3,1},... | collective-permute-start | bytes 196616 | tf_op jit(solution)/shard_map/ppermute | solution.py:18
  28.5 1.4 %collective-permute-start.14 = (bf16[128,256]{1,0:T(8,128)(2,1)S(1)}, bf16[128,256]{1,0:T(8,128)(2,1)S(1)}, u32[]{:S(2)}, u32[]{:S(2)}) collective-permute-start(bf16[128,256]{1,0:T(8,128)(2,1)S(1)} %fusion.37), channel_id=1, source_target_pairs={{0,8},{2,10},{4,12},{6,14},{8,0},{10,2},{12,4},{14,6},{1,9},{3,11}... | collective-permute-start | bytes 196616 | tf_op jit(solution)/shard_map/ppermute | solution.py:18
  29.9 1.7 %collective-permute-start.12 = (bf16[128,256]{1,0:T(8,128)(2,1)S(1)}, bf16[128,256]{1,0:T(8,128)(2,1)S(1)}, u32[]{:S(2)}, u32[]{:S(2)}) collective-permute-start(bf16[128,256]{1,0:T(8,128)(2,1)S(1)} %fusion.36), channel_id=1, source_target_pairs={{0,8},{2,10},{4,12},{6,14},{8,0},{10,2},{12,4},{14,6},{1,9},{3,11}... | collective-permute-start | bytes 196616 | tf_op jit(solution)/shard_map/ppermute | solution.py:18
  32.3 1.1 %collective-permute-start.15 = (bf16[128,512]{1,0:T(8,128)(2,1)S(1)}, bf16[128,512]{1,0:T(8,128)(2,1)S(1)}, u32[]{:S(2)}, u32[]{:S(2)}) collective-permute-start(bf16[128,512]{1,0:T(8,128)(2,1)S(1)} %pad_maximum_fusion.2), channel_id=1, source_target_pairs={{0,4},{2,6},{4,0},{6,2},{8,12},{10,14},{12,8},{14,10},{1,5},{3,7},... | collective-permute-start | bytes 393224 | tf_op jit(solution)/shard_map/ppermute | solution.py:18
  33.4 1.1 %collective-permute-start.11 = (bf16[128,512]{1,0:T(8,128)(2,1)S(1)}, bf16[128,512]{1,0:T(8,128)(2,1)S(1)}, u32[]{:S(2)}, u32[]{:S(2)}) collective-permute-start(bf16[128,512]{1,0:T(8,128)(2,1)S(1)} %pad_maximum_fusion.1), channel_id=1, source_target_pairs={{0,2},{2,0},{4,6},{6,4},{8,10},{10,8},{12,14},{14,12},{1,3},{3,1},... | collective-permute-start | bytes 393224 | tf_op jit(solution)/shard_map/ppermute | solution.py:18
  34.5 1.6 %collective-permute-done.12 = bf16[128,256]{1,0:T(8,128)(2,1)S(1)} collective-permute-done((bf16[128,256]{1,0:T(8,128)(2,1)S(1)}, bf16[128,256]{1,0:T(8,128)(2,1)S(1)}, u32[]{:S(2)}, u32[]{:S(2)}) %collective-permute-start.12) | collective-permute-done | bytes 65568 | tf_op jit(solution)/shard_map/ppermute | solution.py:18
  36.3 1.4 %collective-permute-start.18 = (bf16[128,256]{1,0:T(8,128)(2,1)S(1)}, bf16[128,256]{1,0:T(8,128)(2,1)S(1)}, u32[]{:S(2)}, u32[]{:S(2)}) collective-permute-start(bf16[128,256]{1,0:T(8,128)(2,1)S(1)} %multiply_convert_fusion), channel_id=1, source_target_pairs={{0,2},{2,0},{4,6},{6,4},{8,10},{10,8},{12,14},{14,12},{1,3},{3,1},... | collective-permute-start | bytes 196616 | tf_op jit(solution)/shard_map/ppermute | solution.py:18
  37.7 2.8 %collective-permute-done.16 = bf16[128,256]{1,0:T(8,128)(2,1)S(1)} collective-permute-done((bf16[128,256]{1,0:T(8,128)(2,1)S(1)}, bf16[128,256]{1,0:T(8,128)(2,1)S(1)}, u32[]{:S(2)}, u32[]{:S(2)}) %collective-permute-start.16) | collective-permute-done | bytes 65568 | tf_op jit(solution)/shard_map/ppermute | solution.py:18
  40.6 1.4 %collective-permute-start.17 = (bf16[128,512]{1,0:T(8,128)(2,1)S(1)}, bf16[128,512]{1,0:T(8,128)(2,1)S(1)}, u32[]{:S(2)}, u32[]{:S(2)}) collective-permute-start(bf16[128,512]{1,0:T(8,128)(2,1)S(1)} %pad_maximum_fusion.3), channel_id=1, source_target_pairs={{0,2},{2,0},{4,6},{6,4},{8,10},{10,8},{12,14},{14,12},{1,3},{3,1},... | collective-permute-start | bytes 393224 | tf_op jit(solution)/shard_map/ppermute | solution.py:18
  42.1 2.1 %collective-permute-start.19 = (bf16[128,512]{1,0:T(8,128)(2,1)S(1)}, bf16[128,512]{1,0:T(8,128)(2,1)S(1)}, u32[]{:S(2)}, u32[]{:S(2)}) collective-permute-start(bf16[128,512]{1,0:T(8,128)(2,1)S(1)} %pad_maximum_fusion.4), channel_id=1, source_target_pairs={{0,4},{2,6},{4,0},{6,2},{8,12},{10,14},{12,8},{14,10},{1,5},{3,7},... | collective-permute-start | bytes 393224 | tf_op jit(solution)/shard_map/ppermute | solution.py:18
  45.7 1.4 %collective-permute-done.19 = bf16[128,512]{1,0:T(8,128)(2,1)S(1)} collective-permute-done((bf16[128,512]{1,0:T(8,128)(2,1)S(1)}, bf16[128,512]{1,0:T(8,128)(2,1)S(1)}, u32[]{:S(2)}, u32[]{:S(2)}) %collective-permute-start.19) | collective-permute-done | bytes 131104 | tf_op jit(solution)/shard_map/ppermute | solution.py:18
  48.1 1.5 %collective-permute-done.20.other_ref = f32[512,128]{1,0:T(8,128)S(1)} collective-permute-done((f32[512,128]{1,0:T(8,128)S(1)}, f32[512,128]{1,0:T(8,128)S(1)}, u32[]{:S(2)}, u32[]{:S(2)}) %collective-permute-start.20) | collective-permute-done | bytes 262176 | tf_op jit(solution)/shard_map/ppermute | solution.py:18
  50.1 3.1 %collective-permute-start.24 = (f32[72,128]{1,0:T(8,128)S(1)}, f32[72,128]{1,0:T(8,128)S(1)}, u32[]{:S(2)}, u32[]{:S(2)}) collective-permute-start(f32[72,128]{1,0:T(8,128)S(1)} %make_gram.1), channel_id=1, source_target_pairs={{0,10},{1,15},{2,8},{3,13},{4,14},{5,11},{6,12},{7,9},{8,2},{9,7},... | collective-permute-start | bytes 110600 | tf_op jit(solution)/shard_map/ppermute | solution.py:36
  53.2 1.4 %collective-permute-start.22 = (f32[72,128]{1,0:T(8,128)S(1)}, f32[72,128]{1,0:T(8,128)S(1)}, u32[]{:S(2)}, u32[]{:S(2)}) collective-permute-start(f32[72,128]{1,0:T(8,128)S(1)} %make_gram.1), channel_id=1, source_target_pairs={{0,2},{1,7},{2,0},{3,5},{4,6},{5,3},{6,4},{7,1},{8,10},{9,15},{10,... | collective-permute-start | bytes 110600 | tf_op jit(solution)/shard_map/ppermute | solution.py:36
  55.2 1.5 %collective-permute-done.24 = f32[72,128]{1,0:T(8,128)S(1)} collective-permute-done((f32[72,128]{1,0:T(8,128)S(1)}, f32[72,128]{1,0:T(8,128)S(1)}, u32[]{:S(2)}, u32[]{:S(2)}) %collective-permute-start.24) | collective-permute-done | bytes 36896 | tf_op jit(solution)/shard_map/ppermute | solution.py:36
  56.7 1.4 %collective-permute-done.23 = f32[72,128]{1,0:T(8,128)S(1)} collective-permute-done((f32[72,128]{1,0:T(8,128)S(1)}, f32[72,128]{1,0:T(8,128)S(1)}, u32[]{:S(2)}, u32[]{:S(2)}) %collective-permute-start.23) | collective-permute-done | bytes 36896 | tf_op jit(solution)/shard_map/ppermute | solution.py:36
  58.2 1.1 %collective-permute-start.25 = (f32[72,128]{1,0:T(8,128)S(1)}, f32[72,128]{1,0:T(8,128)S(1)}, u32[]{:S(2)}, u32[]{:S(2)}) collective-permute-start(f32[72,128]{1,0:T(8,128)S(1)} %add_add_fusion), channel_id=1, source_target_pairs={{0,1},{1,0},{2,3},{3,2},{4,5},{5,4},{6,7},{7,6},{8,9},{9,8},{10,11... | collective-permute-start | bytes 110600 | tf_op jit(solution)/shard_map/ppermute | solution.py:18
  59.3 0.9 collective-permute-done.25
  60.1 4.6 %make_basis.1 = (f32[512,128]{1,0:T(8,128)}, f32[128,1024]{1,0:T(8,128)S(1)}, f32[128,1024]{1,0:T(8,128)S(1)}, f32[128,1024]{1,0:T(8,128)S(1)}, f32[128,1024]{1,0:T(8,128)S(1)}) custom-call(f32[72,128]{1,0:T(8,128)S(1)} %add.116.gram_ref, f32[512,128]{1,0:T(8,128)S(1)} %fusion.mine_ref, f32[512,128]{1,0:T(8,128)S(1)} %collective-permute-done.20.other_ref, ...), custom_call_target="tpu_custom_call" | custom-call | tf_op jit(solution)/shard_map/make_basis/pallas_call | solution.py:311
  64.9 0.7 collective-permute-start.26
  65.7 1.8 %collective-permute-start.28 = (bf16[2,2,16,1024]{3,2,0,1:T(8,128)(2,1)S(1)}, bf16[2,2,16,1024]{3,2,0,1:T(8,128)(2,1)S(1)}, u32[]{:S(2)}, u32[]{:S(2)}) collective-permute-start(bf16[2,2,16,1024]{3,2,0,1:T(8,128)(2,1)S(1)} %fusion.19), channel_id=1, source_target_pairs={{0,4},{2,6},{4,0},{6,2},{8,12},{10,14},{12,8},{14,10},{1,5},{3,7},... | collective-permute-start | bytes 393224 | tf_op jit(solution)/shard_map/ppermute | solution.py:18
  67.5 3.2 %collective-permute-done.26 = bf16[2,2,16,1024]{3,2,0,1:T(8,128)(2,1)S(1)} collective-permute-done((bf16[2,2,16,1024]{3,2,0,1:T(8,128)(2,1)S(1)}, bf16[2,2,16,1024]{3,2,0,1:T(8,128)(2,1)S(1)}, u32[]{:S(2)}, u32[]{:S(2)}) %collective-permute-start.26) | collective-permute-done | bytes 131104 | tf_op jit(solution)/shard_map/ppermute | solution.py:18
  70.7 1.8 %collective-permute-start.27 = (bf16[2,16,1024]{2,1,0:T(8,128)(2,1)S(1)}, bf16[2,16,1024]{2,1,0:T(8,128)(2,1)S(1)}, u32[]{:S(2)}, u32[]{:S(2)}) collective-permute-start(bf16[2,16,1024]{2,1,0:T(8,128)(2,1)S(1)} %fusion.22), channel_id=1, source_target_pairs={{0,4},{2,6},{4,0},{6,2},{8,12},{10,14},{12,8},{14,10},{1,5},{3,7},... | collective-permute-start | bytes 196616 | tf_op jit(solution)/shard_map/ppermute | solution.py:18
  73.5 1.2 %collective-permute-start.32 = (bf16[2,2,16,1024]{3,2,0,1:T(8,128)(2,1)S(1)}, bf16[2,2,16,1024]{3,2,0,1:T(8,128)(2,1)S(1)}, u32[]{:S(2)}, u32[]{:S(2)}) collective-permute-start(bf16[2,2,16,1024]{3,2,0,1:T(8,128)(2,1)S(1)} %fusion.21), channel_id=1, source_target_pairs={{0,4},{2,6},{4,0},{6,2},{8,12},{10,14},{12,8},{14,10},{1,5},{3,7},... | collective-permute-start | bytes 393224 | tf_op jit(solution)/shard_map/ppermute | solution.py:18
  75.4 2.3 %collective-permute-done.31 = bf16[2,16,1024]{2,1,0:T(8,128)(2,1)S(1)} collective-permute-done((bf16[2,16,1024]{2,1,0:T(8,128)(2,1)S(1)}, bf16[2,16,1024]{2,1,0:T(8,128)(2,1)S(1)}, u32[]{:S(2)}, u32[]{:S(2)}) %collective-permute-start.31) | collective-permute-done | bytes 65568 | tf_op jit(solution)/shard_map/ppermute | solution.py:18
  77.7 1.0 %collective-permute-start.33 = (bf16[16,1024]{1,0:T(8,128)(2,1)S(1)}, bf16[16,1024]{1,0:T(8,128)(2,1)S(1)}, u32[]{:S(2)}, u32[]{:S(2)}) collective-permute-start(bf16[16,1024]{1,0:T(8,128)(2,1)S(1)} %fusion.31), channel_id=1, source_target_pairs={{0,8},{2,10},{4,12},{6,14},{8,0},{10,2},{12,4},{14,6},{1,9},{3,11}... | collective-permute-start | bytes 98312 | tf_op jit(solution)/shard_map/ppermute | solution.py:18
  78.8 2.0 %collective-permute-start.29 = (bf16[16,1024]{1,0:T(8,128)(2,1)S(1)}, bf16[16,1024]{1,0:T(8,128)(2,1)S(1)}, u32[]{:S(2)}, u32[]{:S(2)}) collective-permute-start(bf16[16,1024]{1,0:T(8,128)(2,1)S(1)} %fusion.30), channel_id=1, source_target_pairs={{0,8},{2,10},{4,12},{6,14},{8,0},{10,2},{12,4},{14,6},{1,9},{3,11}... | collective-permute-start | bytes 98312 | tf_op jit(solution)/shard_map/ppermute | solution.py:18
  81.7 0.8 collective-permute-start.34
  82.7 1.0 %collective-permute-done.29 = bf16[16,1024]{1,0:T(8,128)(2,1)S(1)} collective-permute-done((bf16[16,1024]{1,0:T(8,128)(2,1)S(1)}, bf16[16,1024]{1,0:T(8,128)(2,1)S(1)}, u32[]{:S(2)}, u32[]{:S(2)}) %collective-permute-start.29) | collective-permute-done | bytes 32800 | tf_op jit(solution)/shard_map/ppermute | solution.py:18
  83.7 1.6 %collective-permute-done.36 = bf16[2,16,1024]{2,1,0:T(8,128)(2,1)S(1)} collective-permute-done((bf16[2,16,1024]{2,1,0:T(8,128)(2,1)S(1)}, bf16[2,16,1024]{2,1,0:T(8,128)(2,1)S(1)}, u32[]{:S(2)}, u32[]{:S(2)}) %collective-permute-start.36) | collective-permute-done | bytes 65568 | tf_op jit(solution)/shard_map/ppermute | solution.py:18
  85.3 1.0 %collective-permute-start.37 = (bf16[16,1024]{1,0:T(8,128)(2,1)S(1)}, bf16[16,1024]{1,0:T(8,128)(2,1)S(1)}, u32[]{:S(2)}, u32[]{:S(2)}) collective-permute-start(bf16[16,1024]{1,0:T(8,128)(2,1)S(1)} %fusion.33), channel_id=1, source_target_pairs={{0,8},{2,10},{4,12},{6,14},{8,0},{10,2},{12,4},{14,6},{1,9},{3,11}... | collective-permute-start | bytes 98312 | tf_op jit(solution)/shard_map/ppermute | solution.py:18
  86.4 1.9 %collective-permute-start.35 = (bf16[16,1024]{1,0:T(8,128)(2,1)S(1)}, bf16[16,1024]{1,0:T(8,128)(2,1)S(1)}, u32[]{:S(2)}, u32[]{:S(2)}) collective-permute-start(bf16[16,1024]{1,0:T(8,128)(2,1)S(1)} %fusion.32), channel_id=1, source_target_pairs={{0,8},{2,10},{4,12},{6,14},{8,0},{10,2},{12,4},{14,6},{1,9},{3,11}... | collective-permute-start | bytes 98312 | tf_op jit(solution)/shard_map/ppermute | solution.py:18
  88.4 1.8 %collective-permute-done.37 = bf16[16,1024]{1,0:T(8,128)(2,1)S(1)} collective-permute-done((bf16[16,1024]{1,0:T(8,128)(2,1)S(1)}, bf16[16,1024]{1,0:T(8,128)(2,1)S(1)}, u32[]{:S(2)}, u32[]{:S(2)}) %collective-permute-start.37) | collective-permute-done | bytes 32800 | tf_op jit(solution)/shard_map/ppermute | solution.py:18
  90.2 1.1 %collective-permute-done.35 = bf16[16,1024]{1,0:T(8,128)(2,1)S(1)} collective-permute-done((bf16[16,1024]{1,0:T(8,128)(2,1)S(1)}, bf16[16,1024]{1,0:T(8,128)(2,1)S(1)}, u32[]{:S(2)}, u32[]{:S(2)}) %collective-permute-start.35) | collective-permute-done | bytes 32800 | tf_op jit(solution)/shard_map/ppermute | solution.py:18
  (102 shorter events, 10.5 us)
Async XLA Ops:
  0.6 0.9 copy-start
  4.6 6.6 %collective-permute-start.2 = (bf16[128,512]{1,0:T(8,128)(2,1)S(1)}, bf16[128,512]{1,0:T(8,128)(2,1)S(1)}, u32[]{:S(2)}, u32[]{:S(2)}) collective-permute-start(bf16[128,512]{1,0:T(8,128)(2,1)S(1)} %select_convert_fusion.6), channel_id=1, source_target_pairs={{0,4},{2,6},{4,0},{6,2},{8,12},{10,14},{12,8},{14,10},{1,5},{3,7},... | collective-permute-start | bytes 393224 | tf_op jit(solution)/shard_map/ppermute | solution.py:18
  7.7 5.3 %collective-permute-start = (bf16[128,512]{1,0:T(8,128)(2,1)S(1)}, bf16[128,512]{1,0:T(8,128)(2,1)S(1)}, u32[]{:S(2)}, u32[]{:S(2)}) collective-permute-start(bf16[128,512]{1,0:T(8,128)(2,1)S(1)} %select_convert_fusion.7), channel_id=1, source_target_pairs={{0,2},{2,0},{4,6},{6,4},{8,10},{10,8},{12,14},{14,12},{1,3},{3,1},... | collective-permute-start | bytes 393224 | tf_op jit(solution)/shard_map/ppermute | solution.py:18
  11.3 5.3 %collective-permute-start.5 = (bf16[128,256]{1,0:T(8,128)(2,1)S(1)}, bf16[128,256]{1,0:T(8,128)(2,1)S(1)}, u32[]{:S(2)}, u32[]{:S(2)}) collective-permute-start(bf16[128,256]{1,0:T(8,128)(2,1)S(1)} %select_convert_fusion.14), channel_id=1, source_target_pairs={{0,2},{2,0},{4,6},{6,4},{8,10},{10,8},{12,14},{14,12},{1,3},{3,1},... | collective-permute-start | bytes 196616 | tf_op jit(solution)/shard_map/ppermute | solution.py:18
  13.1 4.9 %collective-permute-start.1 = (bf16[128,256]{1,0:T(8,128)(2,1)S(1)}, bf16[128,256]{1,0:T(8,128)(2,1)S(1)}, u32[]{:S(2)}, u32[]{:S(2)}) collective-permute-start(bf16[128,256]{1,0:T(8,128)(2,1)S(1)} %select_convert_fusion.15), channel_id=1, source_target_pairs={{0,4},{2,6},{4,0},{6,2},{8,12},{10,14},{12,8},{14,10},{1,5},{3,7},... | collective-permute-start | bytes 196616 | tf_op jit(solution)/shard_map/ppermute | solution.py:18
  14.8 6.3 %collective-permute-start.6 = (bf16[128,512]{1,0:T(8,128)(2,1)S(1)}, bf16[128,512]{1,0:T(8,128)(2,1)S(1)}, u32[]{:S(2)}, u32[]{:S(2)}) collective-permute-start(bf16[128,512]{1,0:T(8,128)(2,1)S(1)} %select_convert_fusion.4), channel_id=1, source_target_pairs={{0,4},{2,6},{4,0},{6,2},{8,12},{10,14},{12,8},{14,10},{1,5},{3,7},... | collective-permute-start | bytes 393224 | tf_op jit(solution)/shard_map/ppermute | solution.py:18
  15.3 6.9 %collective-permute-start.4 = (bf16[128,512]{1,0:T(8,128)(2,1)S(1)}, bf16[128,512]{1,0:T(8,128)(2,1)S(1)}, u32[]{:S(2)}, u32[]{:S(2)}) collective-permute-start(bf16[128,512]{1,0:T(8,128)(2,1)S(1)} %select_convert_fusion.5), channel_id=1, source_target_pairs={{0,2},{2,0},{4,6},{6,4},{8,10},{10,8},{12,14},{14,12},{1,3},{3,1},... | collective-permute-start | bytes 393224 | tf_op jit(solution)/shard_map/ppermute | solution.py:18
  18.0 26.3 %copy-start.1 = (bf16[512,4096]{1,0:T(8,128)(2,1)S(1)}, bf16[512,4096]{1,0:T(8,128)(2,1)}, u32[]{:S(2)}) copy-start(bf16[512,4096]{1,0:T(8,128)(2,1)} %slab_ref.3) | copy-start | bytes 12582916
  18.0 6.4 %collective-permute-start.9 = (bf16[128,256]{1,0:T(8,128)(2,1)S(1)}, bf16[128,256]{1,0:T(8,128)(2,1)S(1)}, u32[]{:S(2)}, u32[]{:S(2)}) collective-permute-start(bf16[128,256]{1,0:T(8,128)(2,1)S(1)} %fusion.35), channel_id=1, source_target_pairs={{0,8},{2,10},{4,12},{6,14},{8,0},{10,2},{12,4},{14,6},{1,9},{3,11}... | collective-permute-start | bytes 196616 | tf_op jit(solution)/shard_map/ppermute | solution.py:18
  20.8 5.9 %collective-permute-start.3 = (bf16[128,256]{1,0:T(8,128)(2,1)S(1)}, bf16[128,256]{1,0:T(8,128)(2,1)S(1)}, u32[]{:S(2)}, u32[]{:S(2)}) collective-permute-start(bf16[128,256]{1,0:T(8,128)(2,1)S(1)} %fusion.34), channel_id=1, source_target_pairs={{0,8},{2,10},{4,12},{6,14},{8,0},{10,2},{12,4},{14,6},{1,9},{3,11}... | collective-permute-start | bytes 196616 | tf_op jit(solution)/shard_map/ppermute | solution.py:18
  21.1 7.3 %collective-permute-start.10 = (bf16[128,256]{1,0:T(8,128)(2,1)S(1)}, bf16[128,256]{1,0:T(8,128)(2,1)S(1)}, u32[]{:S(2)}, u32[]{:S(2)}) collective-permute-start(bf16[128,256]{1,0:T(8,128)(2,1)S(1)} %select_convert_fusion.12), channel_id=1, source_target_pairs={{0,2},{2,0},{4,6},{6,4},{8,10},{10,8},{12,14},{14,12},{1,3},{3,1},... | collective-permute-start | bytes 196616 | tf_op jit(solution)/shard_map/ppermute | solution.py:18
  22.3 7.6 %collective-permute-start.8 = (bf16[128,256]{1,0:T(8,128)(2,1)S(1)}, bf16[128,256]{1,0:T(8,128)(2,1)S(1)}, u32[]{:S(2)}, u32[]{:S(2)}) collective-permute-start(bf16[128,256]{1,0:T(8,128)(2,1)S(1)} %select_convert_fusion.13), channel_id=1, source_target_pairs={{0,4},{2,6},{4,0},{6,2},{8,12},{10,14},{12,8},{14,10},{1,5},{3,7},... | collective-permute-start | bytes 196616 | tf_op jit(solution)/shard_map/ppermute | solution.py:18
  26.7 5.5 %collective-permute-start.7 = (bf16[128,256]{1,0:T(8,128)(2,1)S(1)}, bf16[128,256]{1,0:T(8,128)(2,1)S(1)}, u32[]{:S(2)}, u32[]{:S(2)}) collective-permute-start(bf16[128,256]{1,0:T(8,128)(2,1)S(1)} %multiply_convert_fusion.3), channel_id=1, source_target_pairs={{0,4},{2,6},{4,0},{6,2},{8,12},{10,14},{12,8},{14,10},{1,5},{3,7},... | collective-permute-start | bytes 196616 | tf_op jit(solution)/shard_map/ppermute | solution.py:18
  27.4 4.8 %collective-permute-start.13 = (bf16[128,256]{1,0:T(8,128)(2,1)S(1)}, bf16[128,256]{1,0:T(8,128)(2,1)S(1)}, u32[]{:S(2)}, u32[]{:S(2)}) collective-permute-start(bf16[128,256]{1,0:T(8,128)(2,1)S(1)} %multiply_convert_fusion.2), channel_id=1, source_target_pairs={{0,2},{2,0},{4,6},{6,4},{8,10},{10,8},{12,14},{14,12},{1,3},{3,1},... | collective-permute-start | bytes 196616 | tf_op jit(solution)/shard_map/ppermute | solution.py:18
  28.5 6.0 %collective-permute-start.14 = (bf16[128,256]{1,0:T(8,128)(2,1)S(1)}, bf16[128,256]{1,0:T(8,128)(2,1)S(1)}, u32[]{:S(2)}, u32[]{:S(2)}) collective-permute-start(bf16[128,256]{1,0:T(8,128)(2,1)S(1)} %fusion.37), channel_id=1, source_target_pairs={{0,8},{2,10},{4,12},{6,14},{8,0},{10,2},{12,4},{14,6},{1,9},{3,11}... | collective-permute-start | bytes 196616 | tf_op jit(solution)/shard_map/ppermute | solution.py:18
  29.9 6.2 %collective-permute-start.12 = (bf16[128,256]{1,0:T(8,128)(2,1)S(1)}, bf16[128,256]{1,0:T(8,128)(2,1)S(1)}, u32[]{:S(2)}, u32[]{:S(2)}) collective-permute-start(bf16[128,256]{1,0:T(8,128)(2,1)S(1)} %fusion.36), channel_id=1, source_target_pairs={{0,8},{2,10},{4,12},{6,14},{8,0},{10,2},{12,4},{14,6},{1,9},{3,11}... | collective-permute-start | bytes 196616 | tf_op jit(solution)/shard_map/ppermute | solution.py:18
  32.3 11.9 %collective-permute-start.15 = (bf16[128,512]{1,0:T(8,128)(2,1)S(1)}, bf16[128,512]{1,0:T(8,128)(2,1)S(1)}, u32[]{:S(2)}, u32[]{:S(2)}) collective-permute-start(bf16[128,512]{1,0:T(8,128)(2,1)S(1)} %pad_maximum_fusion.2), channel_id=1, source_target_pairs={{0,4},{2,6},{4,0},{6,2},{8,12},{10,14},{12,8},{14,10},{1,5},{3,7},... | collective-permute-start | bytes 393224 | tf_op jit(solution)/shard_map/ppermute | solution.py:18
  33.4 10.8 %collective-permute-start.11 = (bf16[128,512]{1,0:T(8,128)(2,1)S(1)}, bf16[128,512]{1,0:T(8,128)(2,1)S(1)}, u32[]{:S(2)}, u32[]{:S(2)}) collective-permute-start(bf16[128,512]{1,0:T(8,128)(2,1)S(1)} %pad_maximum_fusion.1), channel_id=1, source_target_pairs={{0,2},{2,0},{4,6},{6,4},{8,10},{10,8},{12,14},{14,12},{1,3},{3,1},... | collective-permute-start | bytes 393224 | tf_op jit(solution)/shard_map/ppermute | solution.py:18
  36.1 4.3 %collective-permute-start.16 = (bf16[128,256]{1,0:T(8,128)(2,1)S(1)}, bf16[128,256]{1,0:T(8,128)(2,1)S(1)}, u32[]{:S(2)}, u32[]{:S(2)}) collective-permute-start(bf16[128,256]{1,0:T(8,128)(2,1)S(1)} %multiply_convert_fusion.1), channel_id=1, source_target_pairs={{0,4},{2,6},{4,0},{6,2},{8,12},{10,14},{12,8},{14,10},{1,5},{3,7},... | collective-permute-start | bytes 196616 | tf_op jit(solution)/shard_map/ppermute | solution.py:18
  36.3 4.3 %collective-permute-start.18 = (bf16[128,256]{1,0:T(8,128)(2,1)S(1)}, bf16[128,256]{1,0:T(8,128)(2,1)S(1)}, u32[]{:S(2)}, u32[]{:S(2)}) collective-permute-start(bf16[128,256]{1,0:T(8,128)(2,1)S(1)} %multiply_convert_fusion), channel_id=1, source_target_pairs={{0,2},{2,0},{4,6},{6,4},{8,10},{10,8},{12,14},{14,12},{1,3},{3,1},... | collective-permute-start | bytes 196616 | tf_op jit(solution)/shard_map/ppermute | solution.py:18
  40.6 5.0 %collective-permute-start.17 = (bf16[128,512]{1,0:T(8,128)(2,1)S(1)}, bf16[128,512]{1,0:T(8,128)(2,1)S(1)}, u32[]{:S(2)}, u32[]{:S(2)}) collective-permute-start(bf16[128,512]{1,0:T(8,128)(2,1)S(1)} %pad_maximum_fusion.3), channel_id=1, source_target_pairs={{0,2},{2,0},{4,6},{6,4},{8,10},{10,8},{12,14},{14,12},{1,3},{3,1},... | collective-permute-start | bytes 393224 | tf_op jit(solution)/shard_map/ppermute | solution.py:18
  42.1 5.0 %collective-permute-start.19 = (bf16[128,512]{1,0:T(8,128)(2,1)S(1)}, bf16[128,512]{1,0:T(8,128)(2,1)S(1)}, u32[]{:S(2)}, u32[]{:S(2)}) collective-permute-start(bf16[128,512]{1,0:T(8,128)(2,1)S(1)} %pad_maximum_fusion.4), channel_id=1, source_target_pairs={{0,4},{2,6},{4,0},{6,2},{8,12},{10,14},{12,8},{14,10},{1,5},{3,7},... | collective-permute-start | bytes 393224 | tf_op jit(solution)/shard_map/ppermute | solution.py:18
  48.0 1.6 %collective-permute-start.20 = (f32[512,128]{1,0:T(8,128)S(1)}, f32[512,128]{1,0:T(8,128)S(1)}, u32[]{:S(2)}, u32[]{:S(2)}) collective-permute-start(f32[512,128]{1,0:T(8,128)S(1)} %fusion.mine_ref), channel_id=1, source_target_pairs={{0,1},{1,0},{2,3},{3,2},{4,5},{5,4},{6,7},{7,6},{8,9},{9,8},{10,11... | collective-permute-start | bytes 786440 | tf_op jit(solution)/shard_map/ppermute | solution.py:18
  50.1 6.6 %collective-permute-start.24 = (f32[72,128]{1,0:T(8,128)S(1)}, f32[72,128]{1,0:T(8,128)S(1)}, u32[]{:S(2)}, u32[]{:S(2)}) collective-permute-start(f32[72,128]{1,0:T(8,128)S(1)} %make_gram.1), channel_id=1, source_target_pairs={{0,10},{1,15},{2,8},{3,13},{4,14},{5,11},{6,12},{7,9},{8,2},{9,7},... | collective-permute-start | bytes 110600 | tf_op jit(solution)/shard_map/ppermute | solution.py:36
  53.2 5.0 %collective-permute-start.23 = (f32[72,128]{1,0:T(8,128)S(1)}, f32[72,128]{1,0:T(8,128)S(1)}, u32[]{:S(2)}, u32[]{:S(2)}) collective-permute-start(f32[72,128]{1,0:T(8,128)S(1)} %make_gram.1), channel_id=1, source_target_pairs={{0,8},{1,13},{2,10},{3,15},{4,12},{5,9},{6,14},{7,11},{8,0},{9,5},... | collective-permute-start | bytes 110600 | tf_op jit(solution)/shard_map/ppermute | solution.py:36
  53.2 4.9 %collective-permute-start.22 = (f32[72,128]{1,0:T(8,128)S(1)}, f32[72,128]{1,0:T(8,128)S(1)}, u32[]{:S(2)}, u32[]{:S(2)}) collective-permute-start(f32[72,128]{1,0:T(8,128)S(1)} %make_gram.1), channel_id=1, source_target_pairs={{0,2},{1,7},{2,0},{3,5},{4,6},{5,3},{6,4},{7,1},{8,10},{9,15},{10,... | collective-permute-start | bytes 110600 | tf_op jit(solution)/shard_map/ppermute | solution.py:36
  54.6 3.6 %collective-permute-start.21 = (f32[72,128]{1,0:T(8,128)S(1)}, f32[72,128]{1,0:T(8,128)S(1)}, u32[]{:S(2)}, u32[]{:S(2)}) collective-permute-start(f32[72,128]{1,0:T(8,128)S(1)} %make_gram.1), channel_id=1, source_target_pairs={{1,5},{3,7},{5,1},{7,3},{9,13},{11,15},{13,9},{15,11},{17,21},{19,... | collective-permute-start | bytes 110600 | tf_op jit(solution)/shard_map/ppermute | solution.py:36
  58.2 2.0 %collective-permute-start.25 = (f32[72,128]{1,0:T(8,128)S(1)}, f32[72,128]{1,0:T(8,128)S(1)}, u32[]{:S(2)}, u32[]{:S(2)}) collective-permute-start(f32[72,128]{1,0:T(8,128)S(1)} %add_add_fusion), channel_id=1, source_target_pairs={{0,1},{1,0},{2,3},{3,2},{4,5},{5,4},{6,7},{7,6},{8,9},{9,8},{10,11... | collective-permute-start | bytes 110600 | tf_op jit(solution)/shard_map/ppermute | solution.py:18
  64.9 5.8 %collective-permute-start.26 = (bf16[2,2,16,1024]{3,2,0,1:T(8,128)(2,1)S(1)}, bf16[2,2,16,1024]{3,2,0,1:T(8,128)(2,1)S(1)}, u32[]{:S(2)}, u32[]{:S(2)}) collective-permute-start(bf16[2,2,16,1024]{3,2,0,1:T(8,128)(2,1)S(1)} %fusion.18), channel_id=1, source_target_pairs={{0,2},{2,0},{4,6},{6,4},{8,10},{10,8},{12,14},{14,12},{1,3},{3,1},... | collective-permute-start | bytes 393224 | tf_op jit(solution)/shard_map/ppermute | solution.py:18
  65.7 6.9 %collective-permute-start.28 = (bf16[2,2,16,1024]{3,2,0,1:T(8,128)(2,1)S(1)}, bf16[2,2,16,1024]{3,2,0,1:T(8,128)(2,1)S(1)}, u32[]{:S(2)}, u32[]{:S(2)}) collective-permute-start(bf16[2,2,16,1024]{3,2,0,1:T(8,128)(2,1)S(1)} %fusion.19), channel_id=1, source_target_pairs={{0,4},{2,6},{4,0},{6,2},{8,12},{10,14},{12,8},{14,10},{1,5},{3,7},... | collective-permute-start | bytes 393224 | tf_op jit(solution)/shard_map/ppermute | solution.py:18
  70.7 6.9 %collective-permute-start.27 = (bf16[2,16,1024]{2,1,0:T(8,128)(2,1)S(1)}, bf16[2,16,1024]{2,1,0:T(8,128)(2,1)S(1)}, u32[]{:S(2)}, u32[]{:S(2)}) collective-permute-start(bf16[2,16,1024]{2,1,0:T(8,128)(2,1)S(1)} %fusion.22), channel_id=1, source_target_pairs={{0,4},{2,6},{4,0},{6,2},{8,12},{10,14},{12,8},{14,10},{1,5},{3,7},... | collective-permute-start | bytes 196616 | tf_op jit(solution)/shard_map/ppermute | solution.py:18
  72.6 5.0 %collective-permute-start.31 = (bf16[2,16,1024]{2,1,0:T(8,128)(2,1)S(1)}, bf16[2,16,1024]{2,1,0:T(8,128)(2,1)S(1)}, u32[]{:S(2)}, u32[]{:S(2)}) collective-permute-start(bf16[2,16,1024]{2,1,0:T(8,128)(2,1)S(1)} %fusion.23), channel_id=1, source_target_pairs={{0,2},{2,0},{4,6},{6,4},{8,10},{10,8},{12,14},{14,12},{1,3},{3,1},... | collective-permute-start | bytes 196616 | tf_op jit(solution)/shard_map/ppermute | solution.py:18
  73.5 7.3 %collective-permute-start.32 = (bf16[2,2,16,1024]{3,2,0,1:T(8,128)(2,1)S(1)}, bf16[2,2,16,1024]{3,2,0,1:T(8,128)(2,1)S(1)}, u32[]{:S(2)}, u32[]{:S(2)}) collective-permute-start(bf16[2,2,16,1024]{3,2,0,1:T(8,128)(2,1)S(1)} %fusion.21), channel_id=1, source_target_pairs={{0,4},{2,6},{4,0},{6,2},{8,12},{10,14},{12,8},{14,10},{1,5},{3,7},... | collective-permute-start | bytes 393224 | tf_op jit(solution)/shard_map/ppermute | solution.py:18
  74.7 7.0 %collective-permute-start.30 = (bf16[2,2,16,1024]{3,2,0,1:T(8,128)(2,1)S(1)}, bf16[2,2,16,1024]{3,2,0,1:T(8,128)(2,1)S(1)}, u32[]{:S(2)}, u32[]{:S(2)}) collective-permute-start(bf16[2,2,16,1024]{3,2,0,1:T(8,128)(2,1)S(1)} %fusion.20), channel_id=1, source_target_pairs={{0,2},{2,0},{4,6},{6,4},{8,10},{10,8},{12,14},{14,12},{1,3},{3,1},... | collective-permute-start | bytes 393224 | tf_op jit(solution)/shard_map/ppermute | solution.py:18
  77.7 4.9 %collective-permute-start.33 = (bf16[16,1024]{1,0:T(8,128)(2,1)S(1)}, bf16[16,1024]{1,0:T(8,128)(2,1)S(1)}, u32[]{:S(2)}, u32[]{:S(2)}) collective-permute-start(bf16[16,1024]{1,0:T(8,128)(2,1)S(1)} %fusion.31), channel_id=1, source_target_pairs={{0,8},{2,10},{4,12},{6,14},{8,0},{10,2},{12,4},{14,6},{1,9},{3,11}... | collective-permute-start | bytes 98312 | tf_op jit(solution)/shard_map/ppermute | solution.py:18
  78.8 4.9 %collective-permute-start.29 = (bf16[16,1024]{1,0:T(8,128)(2,1)S(1)}, bf16[16,1024]{1,0:T(8,128)(2,1)S(1)}, u32[]{:S(2)}, u32[]{:S(2)}) collective-permute-start(bf16[16,1024]{1,0:T(8,128)(2,1)S(1)} %fusion.30), channel_id=1, source_target_pairs={{0,8},{2,10},{4,12},{6,14},{8,0},{10,2},{12,4},{14,6},{1,9},{3,11}... | collective-permute-start | bytes 98312 | tf_op jit(solution)/shard_map/ppermute | solution.py:18
  80.9 4.3 %collective-permute-start.36 = (bf16[2,16,1024]{2,1,0:T(8,128)(2,1)S(1)}, bf16[2,16,1024]{2,1,0:T(8,128)(2,1)S(1)}, u32[]{:S(2)}, u32[]{:S(2)}) collective-permute-start(bf16[2,16,1024]{2,1,0:T(8,128)(2,1)S(1)} %fusion.25), channel_id=1, source_target_pairs={{0,2},{2,0},{4,6},{6,4},{8,10},{10,8},{12,14},{14,12},{1,3},{3,1},... | collective-permute-start | bytes 196616 | tf_op jit(solution)/shard_map/ppermute | solution.py:18
  81.7 4.7 %collective-permute-start.34 = (bf16[2,16,1024]{2,1,0:T(8,128)(2,1)S(1)}, bf16[2,16,1024]{2,1,0:T(8,128)(2,1)S(1)}, u32[]{:S(2)}, u32[]{:S(2)}) collective-permute-start(bf16[2,16,1024]{2,1,0:T(8,128)(2,1)S(1)} %fusion.24), channel_id=1, source_target_pairs={{0,4},{2,6},{4,0},{6,2},{8,12},{10,14},{12,8},{14,10},{1,5},{3,7},... | collective-permute-start | bytes 196616 | tf_op jit(solution)/shard_map/ppermute | solution.py:18
  85.3 4.9 %collective-permute-start.37 = (bf16[16,1024]{1,0:T(8,128)(2,1)S(1)}, bf16[16,1024]{1,0:T(8,128)(2,1)S(1)}, u32[]{:S(2)}, u32[]{:S(2)}) collective-permute-start(bf16[16,1024]{1,0:T(8,128)(2,1)S(1)} %fusion.33), channel_id=1, source_target_pairs={{0,8},{2,10},{4,12},{6,14},{8,0},{10,2},{12,4},{14,6},{1,9},{3,11}... | collective-permute-start | bytes 98312 | tf_op jit(solution)/shard_map/ppermute | solution.py:18
  86.4 4.9 %collective-permute-start.35 = (bf16[16,1024]{1,0:T(8,128)(2,1)S(1)}, bf16[16,1024]{1,0:T(8,128)(2,1)S(1)}, u32[]{:S(2)}, u32[]{:S(2)}) collective-permute-start(bf16[16,1024]{1,0:T(8,128)(2,1)S(1)} %fusion.32), channel_id=1, source_target_pairs={{0,8},{2,10},{4,12},{6,14},{8,0},{10,2},{12,4},{14,6},{1,9},{3,11}... | collective-permute-start | bytes 98312 | tf_op jit(solution)/shard_map/ppermute | solution.py:18

commit v20 on v18

--- a/solution.py
+++ b/solution.py
@@ -8,7 +8,7 @@
 from jax.experimental.pallas import tpu as pltpu
 from jax.sharding import PartitionSpec as P
 
-CHUNKS = (1, 1, 3, 3)
+CHUNKS = (1, 2, 1)
 TILE = 512
 KERNEL_VMEM = 50 * 2**20
 

time: 102 us -> 97.7 us (0.958)
  starting transfers between devices: 48.4 us -> 45.3 us
  waiting for transfers between devices: 39.4 us -> 38.3 us
    ppermute x34 -> x26, starting transfers between devices: 43.3 us -> 40.2 us  [swap(): return lax.ppermute(value, axis, [(i, i ^ distance) for i in range(size)])]
    ppermute x34 -> x26, waiting for transfers between devices: 36.7 us -> 35.5 us  [swap(): return lax.ppermute(value, axis, [(i, i ^ distance) for i in range(size)])]
  transfers between devices with their start and end apart: 38 -> 30, of which waited for: 25 -> 19; matrix products, arithmetic and copies ran while one was open for 2% -> 2% of each run, Pallas kernels for 0% -> 0%
where the time goes in v20:
time: 97.7 us; the launch traced here: 97.5 us
  starting transfers between devices  45.3 us (46%)
  waiting for transfers between devices  38.3 us (39%)
  Pallas kernels  8.11 us (8%)
  other arithmetic  2.12 us (2%)
  matrix products  1.59 us (2%)
  local copies, waits for them, and re-layouts  1.06 us (1%)
  between operations  1.02 us (1%)
    ppermute x26, starting transfers between devices, swap(): return lax.ppermute(value, axis, [(i, i ^ distance) for i in range(size)])  40.2 us
    ppermute x26, waiting for transfers between devices, swap(): return lax.ppermute(value, axis, [(i, i ^ distance) for i in range(size)])  35.5 us
    ppermute x4, starting transfers between devices, row_sum(): terms.append(lax.ppermute(value, ('row', 'col'), pairs))  5.1 us
    pallas_call x1, Pallas kernels, make_basis(): pl.pallas_call(functools.partial(basis_kernel, total_cols, root_rows), ou...  4.63 us
    pallas_call x1, Pallas kernels, first_product(): pl.pallas_call(sketch_kernel, out_shape=[jax.ShapeDtypeStruct((width, par...  2.99 us
    ppermute x4, waiting for transfers between devices, row_sum(): terms.append(lax.ppermute(value, ('row', 'col'), pairs))  2.76 us
  transfers between devices with their start and end apart: 30, of which 19 were waited for; matrix products, arithmetic and copies ran while one was open for 2% of the time, Pallas kernels for 0%

profile of v20, /device:TPU:0, one launch (start us, length us, event | category | flops | bytes accessed | tf_op | source)
XLA Modules:
  0.0 97.5 jit_solution(2448236970531508067)
XLA Ops:
  0.6 0.9 copy-done
  1.5 3.0 %first_product.1 = (f32[128,1024]{1,0:T(8,128)S(1)}, f32[128,2048]{1,0:T(8,128)S(1)}, f32[128,1024]{1,0:T(8,128)S(1)}) custom-call(bf16[512,128]{1,0:T(8,128)(2,1)S(1)} %copy-done, bf16[512,4096]{1,0:T(8,128)(2,1)} %slab_ref.3), custom_call_target="tpu_custom_call" | custom-call | flops 536870912 | bytes 4194304 | tf_op jit(solution)/shard_map/first_product/pallas_call | solution.py:133
  4.6 3.0 %collective-permute-start.10 = (bf16[128,512]{1,0:T(8,128)(2,1)S(1)}, bf16[128,512]{1,0:T(8,128)(2,1)S(1)}, u32[]{:S(2)}, u32[]{:S(2)}) collective-permute-start(bf16[128,512]{1,0:T(8,128)(2,1)S(1)} %select_convert_fusion.5), channel_id=1, source_target_pairs={{0,2},{2,0},{4,6},{6,4},{8,10},{10,8},{12,14},{14,12},{1,3},{3,1},... | collective-permute-start | bytes 393224 | tf_op jit(solution)/shard_map/ppermute | solution.py:18
  7.8 2.1 %collective-permute-start.5 = (bf16[128,1024]{1,0:T(8,128)(2,1)S(1)}, bf16[128,1024]{1,0:T(8,128)(2,1)S(1)}, u32[]{:S(2)}, u32[]{:S(2)}) collective-permute-start(bf16[128,1024]{1,0:T(8,128)(2,1)S(1)} %select_convert_fusion.1), channel_id=1, source_target_pairs={{0,4},{2,6},{4,0},{6,2},{8,12},{10,14},{12,8},{14,10},{1,5},{3,7},... | collective-permute-start | bytes 786440 | tf_op jit(solution)/shard_map/ppermute | solution.py:18
  9.9 2.0 %collective-permute-done.10 = bf16[128,512]{1,0:T(8,128)(2,1)S(1)} collective-permute-done((bf16[128,512]{1,0:T(8,128)(2,1)S(1)}, bf16[128,512]{1,0:T(8,128)(2,1)S(1)}, u32[]{:S(2)}, u32[]{:S(2)}) %collective-permute-start.10) | collective-permute-done | bytes 131104 | tf_op jit(solution)/shard_map/ppermute | solution.py:18
  12.0 2.2 %collective-permute-start.11 = (bf16[128,256]{1,0:T(8,128)(2,1)S(1)}, bf16[128,256]{1,0:T(8,128)(2,1)S(1)}, u32[]{:S(2)}, u32[]{:S(2)}) collective-permute-start(bf16[128,256]{1,0:T(8,128)(2,1)S(1)} %select_convert_fusion.11), channel_id=1, source_target_pairs={{0,4},{2,6},{4,0},{6,2},{8,12},{10,14},{12,8},{14,10},{1,5},{3,7},... | collective-permute-start | bytes 196616 | tf_op jit(solution)/shard_map/ppermute | solution.py:18
  14.3 1.6 %collective-permute-start.1 = (bf16[128,256]{1,0:T(8,128)(2,1)S(1)}, bf16[128,256]{1,0:T(8,128)(2,1)S(1)}, u32[]{:S(2)}, u32[]{:S(2)}) collective-permute-start(bf16[128,256]{1,0:T(8,128)(2,1)S(1)} %select_convert_fusion.12), channel_id=1, source_target_pairs={{0,4},{2,6},{4,0},{6,2},{8,12},{10,14},{12,8},{14,10},{1,5},{3,7},... | collective-permute-start | bytes 196616 | tf_op jit(solution)/shard_map/ppermute | solution.py:18
  15.9 1.9 %collective-permute-done.11 = bf16[128,256]{1,0:T(8,128)(2,1)S(1)} collective-permute-done((bf16[128,256]{1,0:T(8,128)(2,1)S(1)}, bf16[128,256]{1,0:T(8,128)(2,1)S(1)}, u32[]{:S(2)}, u32[]{:S(2)}) %collective-permute-start.11) | collective-permute-done | bytes 65568 | tf_op jit(solution)/shard_map/ppermute | solution.py:18
  17.8 2.8 %collective-permute-start.12 = (bf16[128,256]{1,0:T(8,128)(2,1)S(1)}, bf16[128,256]{1,0:T(8,128)(2,1)S(1)}, u32[]{:S(2)}, u32[]{:S(2)}) collective-permute-start(bf16[128,256]{1,0:T(8,128)(2,1)S(1)} %fusion.30), channel_id=1, source_target_pairs={{0,8},{2,10},{4,12},{6,14},{8,0},{10,2},{12,4},{14,6},{1,9},{3,11}... | collective-permute-start | bytes 196616 | tf_op jit(solution)/shard_map/ppermute | solution.py:18
  20.7 1.1 %collective-permute-start.2 = (bf16[128,256]{1,0:T(8,128)(2,1)S(1)}, bf16[128,256]{1,0:T(8,128)(2,1)S(1)}, u32[]{:S(2)}, u32[]{:S(2)}) collective-permute-start(bf16[128,256]{1,0:T(8,128)(2,1)S(1)} %fusion.29), channel_id=1, source_target_pairs={{0,8},{2,10},{4,12},{6,14},{8,0},{10,2},{12,4},{14,6},{1,9},{3,11}... | collective-permute-start | bytes 196616 | tf_op jit(solution)/shard_map/ppermute | solution.py:18
  21.7 2.7 %collective-permute-done.12 = bf16[128,256]{1,0:T(8,128)(2,1)S(1)} collective-permute-done((bf16[128,256]{1,0:T(8,128)(2,1)S(1)}, bf16[128,256]{1,0:T(8,128)(2,1)S(1)}, u32[]{:S(2)}, u32[]{:S(2)}) %collective-permute-start.12) | collective-permute-done | bytes 65568 | tf_op jit(solution)/shard_map/ppermute | solution.py:18
  24.9 1.1 %collective-permute-done.2 = bf16[128,256]{1,0:T(8,128)(2,1)S(1)} collective-permute-done((bf16[128,256]{1,0:T(8,128)(2,1)S(1)}, bf16[128,256]{1,0:T(8,128)(2,1)S(1)}, u32[]{:S(2)}, u32[]{:S(2)}) %collective-permute-start.2) | collective-permute-done | bytes 65568 | tf_op jit(solution)/shard_map/ppermute | solution.py:18
  26.0 1.8 %collective-permute-start.3 = (bf16[128,256]{1,0:T(8,128)(2,1)S(1)}, bf16[128,256]{1,0:T(8,128)(2,1)S(1)}, u32[]{:S(2)}, u32[]{:S(2)}) collective-permute-start(bf16[128,256]{1,0:T(8,128)(2,1)S(1)} %multiply_convert_fusion.2), channel_id=1, source_target_pairs={{0,4},{2,6},{4,0},{6,2},{8,12},{10,14},{12,8},{14,10},{1,5},{3,7},... | collective-permute-start | bytes 196616 | tf_op jit(solution)/shard_map/ppermute | solution.py:18
  28.0 1.6 %collective-permute-start.6 = (bf16[128,512]{1,0:T(8,128)(2,1)S(1)}, bf16[128,512]{1,0:T(8,128)(2,1)S(1)}, u32[]{:S(2)}, u32[]{:S(2)}) collective-permute-start(bf16[128,512]{1,0:T(8,128)(2,1)S(1)} %select_convert_fusion.6), channel_id=1, source_target_pairs={{0,2},{2,0},{4,6},{6,4},{8,10},{10,8},{12,14},{14,12},{1,3},{3,1},... | collective-permute-start | bytes 393224 | tf_op jit(solution)/shard_map/ppermute | solution.py:18
  29.6 1.0 %collective-permute-start.14 = (bf16[128,512]{1,0:T(8,128)(2,1)S(1)}, bf16[128,512]{1,0:T(8,128)(2,1)S(1)}, u32[]{:S(2)}, u32[]{:S(2)}) collective-permute-start(bf16[128,512]{1,0:T(8,128)(2,1)S(1)} %pad_maximum_fusion.3), channel_id=1, source_target_pairs={{0,2},{2,0},{4,6},{6,4},{8,10},{10,8},{12,14},{14,12},{1,3},{3,1},... | collective-permute-start | bytes 393224 | tf_op jit(solution)/shard_map/ppermute | solution.py:18
  30.6 2.5 %collective-permute-done.6 = bf16[128,512]{1,0:T(8,128)(2,1)S(1)} collective-permute-done((bf16[128,512]{1,0:T(8,128)(2,1)S(1)}, bf16[128,512]{1,0:T(8,128)(2,1)S(1)}, u32[]{:S(2)}, u32[]{:S(2)}) %collective-permute-start.6) | collective-permute-done | bytes 131104 | tf_op jit(solution)/shard_map/ppermute | solution.py:18
  33.1 3.1 %collective-permute-start.7 = (bf16[128,512]{1,0:T(8,128)(2,1)S(1)}, bf16[128,512]{1,0:T(8,128)(2,1)S(1)}, u32[]{:S(2)}, u32[]{:S(2)}) collective-permute-start(bf16[128,512]{1,0:T(8,128)(2,1)S(1)} %fusion.28), channel_id=1, source_target_pairs={{0,8},{2,10},{4,12},{6,14},{8,0},{10,2},{12,4},{14,6},{1,9},{3,11}... | collective-permute-start | bytes 393224 | tf_op jit(solution)/shard_map/ppermute | solution.py:18
  36.2 1.6 %collective-permute-start.4 = (bf16[128,512]{1,0:T(8,128)(2,1)S(1)}, bf16[128,512]{1,0:T(8,128)(2,1)S(1)}, u32[]{:S(2)}, u32[]{:S(2)}) collective-permute-start(bf16[128,512]{1,0:T(8,128)(2,1)S(1)} %pad_maximum_fusion.2), channel_id=1, source_target_pairs={{0,2},{2,0},{4,6},{6,4},{8,10},{10,8},{12,14},{14,12},{1,3},{3,1},... | collective-permute-start | bytes 393224 | tf_op jit(solution)/shard_map/ppermute | solution.py:18
  37.8 2.6 %collective-permute-done.7 = bf16[128,512]{1,0:T(8,128)(2,1)S(1)} collective-permute-done((bf16[128,512]{1,0:T(8,128)(2,1)S(1)}, bf16[128,512]{1,0:T(8,128)(2,1)S(1)}, u32[]{:S(2)}, u32[]{:S(2)}) %collective-permute-start.7) | collective-permute-done | bytes 131104 | tf_op jit(solution)/shard_map/ppermute | solution.py:18
  40.5 1.6 %collective-permute-start.8 = (bf16[128,512]{1,0:T(8,128)(2,1)S(1)}, bf16[128,512]{1,0:T(8,128)(2,1)S(1)}, u32[]{:S(2)}, u32[]{:S(2)}) collective-permute-start(bf16[128,512]{1,0:T(8,128)(2,1)S(1)} %multiply_convert_fusion), channel_id=1, source_target_pairs={{0,2},{2,0},{4,6},{6,4},{8,10},{10,8},{12,14},{14,12},{1,3},{3,1},... | collective-permute-start | bytes 393224 | tf_op jit(solution)/shard_map/ppermute | solution.py:18
  42.1 3.4 %collective-permute-done.8 = bf16[128,512]{1,0:T(8,128)(2,1)S(1)} collective-permute-done((bf16[128,512]{1,0:T(8,128)(2,1)S(1)}, bf16[128,512]{1,0:T(8,128)(2,1)S(1)}, u32[]{:S(2)}, u32[]{:S(2)}) %collective-permute-start.8) | collective-permute-done | bytes 131104 | tf_op jit(solution)/shard_map/ppermute | solution.py:18
  46.2 5.8 %collective-permute-done.9 = bf16[128,1024]{1,0:T(8,128)(2,1)S(1)} collective-permute-done((bf16[128,1024]{1,0:T(8,128)(2,1)S(1)}, bf16[128,1024]{1,0:T(8,128)(2,1)S(1)}, u32[]{:S(2)}, u32[]{:S(2)}) %collective-permute-start.9) | collective-permute-done | bytes 262176 | tf_op jit(solution)/shard_map/ppermute | solution.py:18
  52.1 0.7 fusion
  53.4 1.5 %collective-permute-done.15.other_ref = f32[512,128]{1,0:T(8,128)S(1)} collective-permute-done((f32[512,128]{1,0:T(8,128)S(1)}, f32[512,128]{1,0:T(8,128)S(1)}, u32[]{:S(2)}, u32[]{:S(2)}) %collective-permute-start.15) | collective-permute-done | bytes 262176 | tf_op jit(solution)/shard_map/ppermute | solution.py:18
  54.9 0.5 make_gram.1
  55.4 2.9 %collective-permute-start.19 = (f32[72,128]{1,0:T(8,128)S(1)}, f32[72,128]{1,0:T(8,128)S(1)}, u32[]{:S(2)}, u32[]{:S(2)}) collective-permute-start(f32[72,128]{1,0:T(8,128)S(1)} %make_gram.1), channel_id=1, source_target_pairs={{0,10},{1,15},{2,8},{3,13},{4,14},{5,11},{6,12},{7,9},{8,2},{9,7},... | collective-permute-start | bytes 110600 | tf_op jit(solution)/shard_map/ppermute | solution.py:36
  58.3 1.0 %collective-permute-start.18 = (f32[72,128]{1,0:T(8,128)S(1)}, f32[72,128]{1,0:T(8,128)S(1)}, u32[]{:S(2)}, u32[]{:S(2)}) collective-permute-start(f32[72,128]{1,0:T(8,128)S(1)} %make_gram.1), channel_id=1, source_target_pairs={{0,8},{1,13},{2,10},{3,15},{4,12},{5,9},{6,14},{7,11},{8,0},{9,5},... | collective-permute-start | bytes 110600 | tf_op jit(solution)/shard_map/ppermute | solution.py:36
  59.3 0.5 collective-permute-start.17
  59.9 0.7 collective-permute-start.16
  60.5 1.5 %collective-permute-done.19 = f32[72,128]{1,0:T(8,128)S(1)} collective-permute-done((f32[72,128]{1,0:T(8,128)S(1)}, f32[72,128]{1,0:T(8,128)S(1)}, u32[]{:S(2)}, u32[]{:S(2)}) %collective-permute-start.19) | collective-permute-done | bytes 36896 | tf_op jit(solution)/shard_map/ppermute | solution.py:36
  62.0 1.2 %collective-permute-done.18 = f32[72,128]{1,0:T(8,128)S(1)} collective-permute-done((f32[72,128]{1,0:T(8,128)S(1)}, f32[72,128]{1,0:T(8,128)S(1)}, u32[]{:S(2)}, u32[]{:S(2)}) %collective-permute-start.18) | collective-permute-done | bytes 36896 | tf_op jit(solution)/shard_map/ppermute | solution.py:36
  63.3 1.3 %collective-permute-start.20 = (f32[72,128]{1,0:T(8,128)S(1)}, f32[72,128]{1,0:T(8,128)S(1)}, u32[]{:S(2)}, u32[]{:S(2)}) collective-permute-start(f32[72,128]{1,0:T(8,128)S(1)} %add_add_fusion), channel_id=1, source_target_pairs={{0,1},{1,0},{2,3},{3,2},{4,5},{5,4},{6,7},{7,6},{8,9},{9,8},{10,11... | collective-permute-start | bytes 110600 | tf_op jit(solution)/shard_map/ppermute | solution.py:18
  64.6 0.9 collective-permute-done.20
  65.4 4.6 %make_basis.1 = (f32[512,128]{1,0:T(8,128)}, f32[128,1024]{1,0:T(8,128)S(1)}, f32[128,2048]{1,0:T(8,128)S(1)}, f32[128,1024]{1,0:T(8,128)S(1)}) custom-call(f32[72,128]{1,0:T(8,128)S(1)} %add.90.gram_ref, f32[512,128]{1,0:T(8,128)S(1)} %fusion.3.mine_ref, f32[512,128]{1,0:T(8,128)S(1)} %collective-permute-done.15.other_ref, bf16[512,4096]{1,0:T(8,128)(2,1)} %slab_ref.3), custom_call_target="tpu_custom_call" | custom-call | tf_op jit(solution)/shard_map/make_basis/pallas_call | solution.py:294
  70.2 1.5 %collective-permute-start.21 = (bf16[2,2,16,1024]{3,2,0,1:T(8,128)(2,1)S(1)}, bf16[2,2,16,1024]{3,2,0,1:T(8,128)(2,1)S(1)}, u32[]{:S(2)}, u32[]{:S(2)}) collective-permute-start(bf16[2,2,16,1024]{3,2,0,1:T(8,128)(2,1)S(1)} %fusion.17), channel_id=1, source_target_pairs={{0,2},{2,0},{4,6},{6,4},{8,10},{10,8},{12,14},{14,12},{1,3},{3,1},... | collective-permute-start | bytes 393224 | tf_op jit(solution)/shard_map/ppermute | solution.py:18
  71.8 0.6 collective-permute-start.27
  72.5 1.8 %collective-permute-start.24 = (bf16[2,2,16,2048]{3,2,0,1:T(8,128)(2,1)S(1)}, bf16[2,2,16,2048]{3,2,0,1:T(8,128)(2,1)S(1)}, u32[]{:S(2)}, u32[]{:S(2)}) collective-permute-start(bf16[2,2,16,2048]{3,2,0,1:T(8,128)(2,1)S(1)} %fusion.10), channel_id=1, source_target_pairs={{0,4},{2,6},{4,0},{6,2},{8,12},{10,14},{12,8},{14,10},{1,5},{3,7},... | collective-permute-start | bytes 786440 | tf_op jit(solution)/shard_map/ppermute | solution.py:18
  74.3 2.2 %collective-permute-done.21 = bf16[2,2,16,1024]{3,2,0,1:T(8,128)(2,1)S(1)} collective-permute-done((bf16[2,2,16,1024]{3,2,0,1:T(8,128)(2,1)S(1)}, bf16[2,2,16,1024]{3,2,0,1:T(8,128)(2,1)S(1)}, u32[]{:S(2)}, u32[]{:S(2)}) %collective-permute-start.21) | collective-permute-done | bytes 131104 | tf_op jit(solution)/shard_map/ppermute | solution.py:18
  76.6 1.8 %collective-permute-start.22 = (bf16[2,16,1024]{2,1,0:T(8,128)(2,1)S(1)}, bf16[2,16,1024]{2,1,0:T(8,128)(2,1)S(1)}, u32[]{:S(2)}, u32[]{:S(2)}) collective-permute-start(bf16[2,16,1024]{2,1,0:T(8,128)(2,1)S(1)} %fusion.21), channel_id=1, source_target_pairs={{0,4},{2,6},{4,0},{6,2},{8,12},{10,14},{12,8},{14,10},{1,5},{3,7},... | collective-permute-start | bytes 196616 | tf_op jit(solution)/shard_map/ppermute | solution.py:18
  78.8 1.8 %collective-permute-start.28 = (bf16[2,16,1024]{2,1,0:T(8,128)(2,1)S(1)}, bf16[2,16,1024]{2,1,0:T(8,128)(2,1)S(1)}, u32[]{:S(2)}, u32[]{:S(2)}) collective-permute-start(bf16[2,16,1024]{2,1,0:T(8,128)(2,1)S(1)} %fusion.23), channel_id=1, source_target_pairs={{0,4},{2,6},{4,0},{6,2},{8,12},{10,14},{12,8},{14,10},{1,5},{3,7},... | collective-permute-start | bytes 196616 | tf_op jit(solution)/shard_map/ppermute | solution.py:18
  80.6 2.1 %collective-permute-done.22 = bf16[2,16,1024]{2,1,0:T(8,128)(2,1)S(1)} collective-permute-done((bf16[2,16,1024]{2,1,0:T(8,128)(2,1)S(1)}, bf16[2,16,1024]{2,1,0:T(8,128)(2,1)S(1)}, u32[]{:S(2)}, u32[]{:S(2)}) %collective-permute-start.22) | collective-permute-done | bytes 65568 | tf_op jit(solution)/shard_map/ppermute | solution.py:18
  82.7 2.8 %collective-permute-start.23 = (bf16[16,1024]{1,0:T(8,128)(2,1)S(1)}, bf16[16,1024]{1,0:T(8,128)(2,1)S(1)}, u32[]{:S(2)}, u32[]{:S(2)}) collective-permute-start(bf16[16,1024]{1,0:T(8,128)(2,1)S(1)} %fusion.26), channel_id=1, source_target_pairs={{0,8},{2,10},{4,12},{6,14},{8,0},{10,2},{12,4},{14,6},{1,9},{3,11}... | collective-permute-start | bytes 98312 | tf_op jit(solution)/shard_map/ppermute | solution.py:18
  85.6 0.7 collective-permute-start.29
  86.4 1.5 %collective-permute-start.25 = (bf16[2,16,2048]{2,1,0:T(8,128)(2,1)S(1)}, bf16[2,16,2048]{2,1,0:T(8,128)(2,1)S(1)}, u32[]{:S(2)}, u32[]{:S(2)}) collective-permute-start(bf16[2,16,2048]{2,1,0:T(8,128)(2,1)S(1)} %fusion.18), channel_id=1, source_target_pairs={{0,2},{2,0},{4,6},{6,4},{8,10},{10,8},{12,14},{14,12},{1,3},{3,1},... | collective-permute-start | bytes 393224 | tf_op jit(solution)/shard_map/ppermute | solution.py:18
  88.2 3.2 %collective-permute-done.25 = bf16[2,16,2048]{2,1,0:T(8,128)(2,1)S(1)} collective-permute-done((bf16[2,16,2048]{2,1,0:T(8,128)(2,1)S(1)}, bf16[2,16,2048]{2,1,0:T(8,128)(2,1)S(1)}, u32[]{:S(2)}, u32[]{:S(2)}) %collective-permute-start.25) | collective-permute-done | bytes 131104 | tf_op jit(solution)/shard_map/ppermute | solution.py:18
  91.5 2.4 %collective-permute-start.26 = (bf16[16,2048]{1,0:T(8,128)(2,1)S(1)}, bf16[16,2048]{1,0:T(8,128)(2,1)S(1)}, u32[]{:S(2)}, u32[]{:S(2)}) collective-permute-start(bf16[16,2048]{1,0:T(8,128)(2,1)S(1)} %fusion.22), channel_id=1, source_target_pairs={{0,8},{2,10},{4,12},{6,14},{8,0},{10,2},{12,4},{14,6},{1,9},{3,11}... | collective-permute-start | bytes 196616 | tf_op jit(solution)/shard_map/ppermute | solution.py:18
  93.9 2.8 %collective-permute-done.26 = bf16[16,2048]{1,0:T(8,128)(2,1)S(1)} collective-permute-done((bf16[16,2048]{1,0:T(8,128)(2,1)S(1)}, bf16[16,2048]{1,0:T(8,128)(2,1)S(1)}, u32[]{:S(2)}, u32[]{:S(2)}) %collective-permute-start.26) | collective-permute-done | bytes 65568 | tf_op jit(solution)/shard_map/ppermute | solution.py:18
  96.8 0.7 pad_maximum_fusion.1
  (70 shorter events, 3.8 us)
Async XLA Ops:
  0.6 0.9 copy-start
  4.6 7.3 %collective-permute-start.10 = (bf16[128,512]{1,0:T(8,128)(2,1)S(1)}, bf16[128,512]{1,0:T(8,128)(2,1)S(1)}, u32[]{:S(2)}, u32[]{:S(2)}) collective-permute-start(bf16[128,512]{1,0:T(8,128)(2,1)S(1)} %select_convert_fusion.5), channel_id=1, source_target_pairs={{0,2},{2,0},{4,6},{6,4},{8,10},{10,8},{12,14},{14,12},{1,3},{3,1},... | collective-permute-start | bytes 393224 | tf_op jit(solution)/shard_map/ppermute | solution.py:18
  7.6 6.6 %collective-permute-start = (bf16[128,512]{1,0:T(8,128)(2,1)S(1)}, bf16[128,512]{1,0:T(8,128)(2,1)S(1)}, u32[]{:S(2)}, u32[]{:S(2)}) collective-permute-start(bf16[128,512]{1,0:T(8,128)(2,1)S(1)} %select_convert_fusion.7), channel_id=1, source_target_pairs={{0,2},{2,0},{4,6},{6,4},{8,10},{10,8},{12,14},{14,12},{1,3},{3,1},... | collective-permute-start | bytes 393224 | tf_op jit(solution)/shard_map/ppermute | solution.py:18
  7.8 20.1 %collective-permute-start.5 = (bf16[128,1024]{1,0:T(8,128)(2,1)S(1)}, bf16[128,1024]{1,0:T(8,128)(2,1)S(1)}, u32[]{:S(2)}, u32[]{:S(2)}) collective-permute-start(bf16[128,1024]{1,0:T(8,128)(2,1)S(1)} %select_convert_fusion.1), channel_id=1, source_target_pairs={{0,4},{2,6},{4,0},{6,2},{8,12},{10,14},{12,8},{14,10},{1,5},{3,7},... | collective-permute-start | bytes 786440 | tf_op jit(solution)/shard_map/ppermute | solution.py:18
  12.0 5.8 %collective-permute-start.11 = (bf16[128,256]{1,0:T(8,128)(2,1)S(1)}, bf16[128,256]{1,0:T(8,128)(2,1)S(1)}, u32[]{:S(2)}, u32[]{:S(2)}) collective-permute-start(bf16[128,256]{1,0:T(8,128)(2,1)S(1)} %select_convert_fusion.11), channel_id=1, source_target_pairs={{0,4},{2,6},{4,0},{6,2},{8,12},{10,14},{12,8},{14,10},{1,5},{3,7},... | collective-permute-start | bytes 196616 | tf_op jit(solution)/shard_map/ppermute | solution.py:18
  14.3 6.4 %collective-permute-start.1 = (bf16[128,256]{1,0:T(8,128)(2,1)S(1)}, bf16[128,256]{1,0:T(8,128)(2,1)S(1)}, u32[]{:S(2)}, u32[]{:S(2)}) collective-permute-start(bf16[128,256]{1,0:T(8,128)(2,1)S(1)} %select_convert_fusion.12), channel_id=1, source_target_pairs={{0,4},{2,6},{4,0},{6,2},{8,12},{10,14},{12,8},{14,10},{1,5},{3,7},... | collective-permute-start | bytes 196616 | tf_op jit(solution)/shard_map/ppermute | solution.py:18
  17.8 27.9 %copy-start.1 = (bf16[512,4096]{1,0:T(8,128)(2,1)S(1)}, bf16[512,4096]{1,0:T(8,128)(2,1)}, u32[]{:S(2)}) copy-start(bf16[512,4096]{1,0:T(8,128)(2,1)} %slab_ref.3) | copy-start | bytes 12582916
  17.8 6.6 %collective-permute-start.12 = (bf16[128,256]{1,0:T(8,128)(2,1)S(1)}, bf16[128,256]{1,0:T(8,128)(2,1)S(1)}, u32[]{:S(2)}, u32[]{:S(2)}) collective-permute-start(bf16[128,256]{1,0:T(8,128)(2,1)S(1)} %fusion.30), channel_id=1, source_target_pairs={{0,8},{2,10},{4,12},{6,14},{8,0},{10,2},{12,4},{14,6},{1,9},{3,11}... | collective-permute-start | bytes 196616 | tf_op jit(solution)/shard_map/ppermute | solution.py:18
  20.7 5.3 %collective-permute-start.2 = (bf16[128,256]{1,0:T(8,128)(2,1)S(1)}, bf16[128,256]{1,0:T(8,128)(2,1)S(1)}, u32[]{:S(2)}, u32[]{:S(2)}) collective-permute-start(bf16[128,256]{1,0:T(8,128)(2,1)S(1)} %fusion.29), channel_id=1, source_target_pairs={{0,8},{2,10},{4,12},{6,14},{8,0},{10,2},{12,4},{14,6},{1,9},{3,11}... | collective-permute-start | bytes 196616 | tf_op jit(solution)/shard_map/ppermute | solution.py:18
  24.5 5.1 %collective-permute-start.13 = (bf16[128,256]{1,0:T(8,128)(2,1)S(1)}, bf16[128,256]{1,0:T(8,128)(2,1)S(1)}, u32[]{:S(2)}, u32[]{:S(2)}) collective-permute-start(bf16[128,256]{1,0:T(8,128)(2,1)S(1)} %multiply_convert_fusion.1), channel_id=1, source_target_pairs={{0,4},{2,6},{4,0},{6,2},{8,12},{10,14},{12,8},{14,10},{1,5},{3,7},... | collective-permute-start | bytes 196616 | tf_op jit(solution)/shard_map/ppermute | solution.py:18
  26.0 10.2 %collective-permute-start.3 = (bf16[128,256]{1,0:T(8,128)(2,1)S(1)}, bf16[128,256]{1,0:T(8,128)(2,1)S(1)}, u32[]{:S(2)}, u32[]{:S(2)}) collective-permute-start(bf16[128,256]{1,0:T(8,128)(2,1)S(1)} %multiply_convert_fusion.2), channel_id=1, source_target_pairs={{0,4},{2,6},{4,0},{6,2},{8,12},{10,14},{12,8},{14,10},{1,5},{3,7},... | collective-permute-start | bytes 196616 | tf_op jit(solution)/shard_map/ppermute | solution.py:18
  28.0 5.0 %collective-permute-start.6 = (bf16[128,512]{1,0:T(8,128)(2,1)S(1)}, bf16[128,512]{1,0:T(8,128)(2,1)S(1)}, u32[]{:S(2)}, u32[]{:S(2)}) collective-permute-start(bf16[128,512]{1,0:T(8,128)(2,1)S(1)} %select_convert_fusion.6), channel_id=1, source_target_pairs={{0,2},{2,0},{4,6},{6,4},{8,10},{10,8},{12,14},{14,12},{1,3},{3,1},... | collective-permute-start | bytes 393224 | tf_op jit(solution)/shard_map/ppermute | solution.py:18
  29.6 12.5 %collective-permute-start.14 = (bf16[128,512]{1,0:T(8,128)(2,1)S(1)}, bf16[128,512]{1,0:T(8,128)(2,1)S(1)}, u32[]{:S(2)}, u32[]{:S(2)}) collective-permute-start(bf16[128,512]{1,0:T(8,128)(2,1)S(1)} %pad_maximum_fusion.3), channel_id=1, source_target_pairs={{0,2},{2,0},{4,6},{6,4},{8,10},{10,8},{12,14},{14,12},{1,3},{3,1},... | collective-permute-start | bytes 393224 | tf_op jit(solution)/shard_map/ppermute | solution.py:18
  33.1 7.3 %collective-permute-start.7 = (bf16[128,512]{1,0:T(8,128)(2,1)S(1)}, bf16[128,512]{1,0:T(8,128)(2,1)S(1)}, u32[]{:S(2)}, u32[]{:S(2)}) collective-permute-start(bf16[128,512]{1,0:T(8,128)(2,1)S(1)} %fusion.28), channel_id=1, source_target_pairs={{0,8},{2,10},{4,12},{6,14},{8,0},{10,2},{12,4},{14,6},{1,9},{3,11}... | collective-permute-start | bytes 393224 | tf_op jit(solution)/shard_map/ppermute | solution.py:18
  36.2 9.4 %collective-permute-start.4 = (bf16[128,512]{1,0:T(8,128)(2,1)S(1)}, bf16[128,512]{1,0:T(8,128)(2,1)S(1)}, u32[]{:S(2)}, u32[]{:S(2)}) collective-permute-start(bf16[128,512]{1,0:T(8,128)(2,1)S(1)} %pad_maximum_fusion.2), channel_id=1, source_target_pairs={{0,2},{2,0},{4,6},{6,4},{8,10},{10,8},{12,14},{14,12},{1,3},{3,1},... | collective-permute-start | bytes 393224 | tf_op jit(solution)/shard_map/ppermute | solution.py:18
  40.5 5.0 %collective-permute-start.8 = (bf16[128,512]{1,0:T(8,128)(2,1)S(1)}, bf16[128,512]{1,0:T(8,128)(2,1)S(1)}, u32[]{:S(2)}, u32[]{:S(2)}) collective-permute-start(bf16[128,512]{1,0:T(8,128)(2,1)S(1)} %multiply_convert_fusion), channel_id=1, source_target_pairs={{0,2},{2,0},{4,6},{6,4},{8,10},{10,8},{12,14},{14,12},{1,3},{3,1},... | collective-permute-start | bytes 393224 | tf_op jit(solution)/shard_map/ppermute | solution.py:18
  45.6 6.4 %collective-permute-start.9 = (bf16[128,1024]{1,0:T(8,128)(2,1)S(1)}, bf16[128,1024]{1,0:T(8,128)(2,1)S(1)}, u32[]{:S(2)}, u32[]{:S(2)}) collective-permute-start(bf16[128,1024]{1,0:T(8,128)(2,1)S(1)} %pad_maximum_fusion), channel_id=1, source_target_pairs={{0,4},{2,6},{4,0},{6,2},{8,12},{10,14},{12,8},{14,10},{1,5},{3,7},... | collective-permute-start | bytes 786440 | tf_op jit(solution)/shard_map/ppermute | solution.py:18
  53.3 1.6 %collective-permute-start.15 = (f32[512,128]{1,0:T(8,128)S(1)}, f32[512,128]{1,0:T(8,128)S(1)}, u32[]{:S(2)}, u32[]{:S(2)}) collective-permute-start(f32[512,128]{1,0:T(8,128)S(1)} %fusion.3.mine_ref), channel_id=1, source_target_pairs={{0,1},{1,0},{2,3},{3,2},{4,5},{5,4},{6,7},{7,6},{8,9},{9,8},{10,11... | collective-permute-start | bytes 786440 | tf_op jit(solution)/shard_map/ppermute | solution.py:18
  55.4 6.6 %collective-permute-start.19 = (f32[72,128]{1,0:T(8,128)S(1)}, f32[72,128]{1,0:T(8,128)S(1)}, u32[]{:S(2)}, u32[]{:S(2)}) collective-permute-start(f32[72,128]{1,0:T(8,128)S(1)} %make_gram.1), channel_id=1, source_target_pairs={{0,10},{1,15},{2,8},{3,13},{4,14},{5,11},{6,12},{7,9},{8,2},{9,7},... | collective-permute-start | bytes 110600 | tf_op jit(solution)/shard_map/ppermute | solution.py:36
  58.3 4.9 %collective-permute-start.18 = (f32[72,128]{1,0:T(8,128)S(1)}, f32[72,128]{1,0:T(8,128)S(1)}, u32[]{:S(2)}, u32[]{:S(2)}) collective-permute-start(f32[72,128]{1,0:T(8,128)S(1)} %make_gram.1), channel_id=1, source_target_pairs={{0,8},{1,13},{2,10},{3,15},{4,12},{5,9},{6,14},{7,11},{8,0},{9,5},... | collective-permute-start | bytes 110600 | tf_op jit(solution)/shard_map/ppermute | solution.py:36
  59.3 4.0 %collective-permute-start.17 = (f32[72,128]{1,0:T(8,128)S(1)}, f32[72,128]{1,0:T(8,128)S(1)}, u32[]{:S(2)}, u32[]{:S(2)}) collective-permute-start(f32[72,128]{1,0:T(8,128)S(1)} %make_gram.1), channel_id=1, source_target_pairs={{0,2},{1,7},{2,0},{3,5},{4,6},{5,3},{6,4},{7,1},{8,10},{9,15},{10,... | collective-permute-start | bytes 110600 | tf_op jit(solution)/shard_map/ppermute | solution.py:36
  59.9 3.4 %collective-permute-start.16 = (f32[72,128]{1,0:T(8,128)S(1)}, f32[72,128]{1,0:T(8,128)S(1)}, u32[]{:S(2)}, u32[]{:S(2)}) collective-permute-start(f32[72,128]{1,0:T(8,128)S(1)} %make_gram.1), channel_id=1, source_target_pairs={{1,5},{3,7},{5,1},{7,3},{9,13},{11,15},{13,9},{15,11},{17,21},{19,... | collective-permute-start | bytes 110600 | tf_op jit(solution)/shard_map/ppermute | solution.py:36
  63.3 2.1 %collective-permute-start.20 = (f32[72,128]{1,0:T(8,128)S(1)}, f32[72,128]{1,0:T(8,128)S(1)}, u32[]{:S(2)}, u32[]{:S(2)}) collective-permute-start(f32[72,128]{1,0:T(8,128)S(1)} %add_add_fusion), channel_id=1, source_target_pairs={{0,1},{1,0},{2,3},{3,2},{4,5},{5,4},{6,7},{7,6},{8,9},{9,8},{10,11... | collective-permute-start | bytes 110600 | tf_op jit(solution)/shard_map/ppermute | solution.py:18
  70.2 6.4 %collective-permute-start.21 = (bf16[2,2,16,1024]{3,2,0,1:T(8,128)(2,1)S(1)}, bf16[2,2,16,1024]{3,2,0,1:T(8,128)(2,1)S(1)}, u32[]{:S(2)}, u32[]{:S(2)}) collective-permute-start(bf16[2,2,16,1024]{3,2,0,1:T(8,128)(2,1)S(1)} %fusion.17), channel_id=1, source_target_pairs={{0,2},{2,0},{4,6},{6,4},{8,10},{10,8},{12,14},{14,12},{1,3},{3,1},... | collective-permute-start | bytes 393224 | tf_op jit(solution)/shard_map/ppermute | solution.py:18
  71.8 7.0 %collective-permute-start.27 = (bf16[2,2,16,1024]{3,2,0,1:T(8,128)(2,1)S(1)}, bf16[2,2,16,1024]{3,2,0,1:T(8,128)(2,1)S(1)}, u32[]{:S(2)}, u32[]{:S(2)}) collective-permute-start(bf16[2,2,16,1024]{3,2,0,1:T(8,128)(2,1)S(1)} %fusion.19), channel_id=1, source_target_pairs={{0,2},{2,0},{4,6},{6,4},{8,10},{10,8},{12,14},{14,12},{1,3},{3,1},... | collective-permute-start | bytes 393224 | tf_op jit(solution)/shard_map/ppermute | solution.py:18
  72.5 13.8 %collective-permute-start.24 = (bf16[2,2,16,2048]{3,2,0,1:T(8,128)(2,1)S(1)}, bf16[2,2,16,2048]{3,2,0,1:T(8,128)(2,1)S(1)}, u32[]{:S(2)}, u32[]{:S(2)}) collective-permute-start(bf16[2,2,16,2048]{3,2,0,1:T(8,128)(2,1)S(1)} %fusion.10), channel_id=1, source_target_pairs={{0,4},{2,6},{4,0},{6,2},{8,12},{10,14},{12,8},{14,10},{1,5},{3,7},... | collective-permute-start | bytes 786440 | tf_op jit(solution)/shard_map/ppermute | solution.py:18
  76.6 6.1 %collective-permute-start.22 = (bf16[2,16,1024]{2,1,0:T(8,128)(2,1)S(1)}, bf16[2,16,1024]{2,1,0:T(8,128)(2,1)S(1)}, u32[]{:S(2)}, u32[]{:S(2)}) collective-permute-start(bf16[2,16,1024]{2,1,0:T(8,128)(2,1)S(1)} %fusion.21), channel_id=1, source_target_pairs={{0,4},{2,6},{4,0},{6,2},{8,12},{10,14},{12,8},{14,10},{1,5},{3,7},... | collective-permute-start | bytes 196616 | tf_op jit(solution)/shard_map/ppermute | solution.py:18
  78.8 6.8 %collective-permute-start.28 = (bf16[2,16,1024]{2,1,0:T(8,128)(2,1)S(1)}, bf16[2,16,1024]{2,1,0:T(8,128)(2,1)S(1)}, u32[]{:S(2)}, u32[]{:S(2)}) collective-permute-start(bf16[2,16,1024]{2,1,0:T(8,128)(2,1)S(1)} %fusion.23), channel_id=1, source_target_pairs={{0,4},{2,6},{4,0},{6,2},{8,12},{10,14},{12,8},{14,10},{1,5},{3,7},... | collective-permute-start | bytes 196616 | tf_op jit(solution)/shard_map/ppermute | solution.py:18
  82.7 5.4 %collective-permute-start.23 = (bf16[16,1024]{1,0:T(8,128)(2,1)S(1)}, bf16[16,1024]{1,0:T(8,128)(2,1)S(1)}, u32[]{:S(2)}, u32[]{:S(2)}) collective-permute-start(bf16[16,1024]{1,0:T(8,128)(2,1)S(1)} %fusion.26), channel_id=1, source_target_pairs={{0,8},{2,10},{4,12},{6,14},{8,0},{10,2},{12,4},{14,6},{1,9},{3,11}... | collective-permute-start | bytes 98312 | tf_op jit(solution)/shard_map/ppermute | solution.py:18
  85.6 8.3 %collective-permute-start.29 = (bf16[16,1024]{1,0:T(8,128)(2,1)S(1)}, bf16[16,1024]{1,0:T(8,128)(2,1)S(1)}, u32[]{:S(2)}, u32[]{:S(2)}) collective-permute-start(bf16[16,1024]{1,0:T(8,128)(2,1)S(1)} %fusion.27), channel_id=1, source_target_pairs={{0,8},{2,10},{4,12},{6,14},{8,0},{10,2},{12,4},{14,6},{1,9},{3,11}... | collective-permute-start | bytes 98312 | tf_op jit(solution)/shard_map/ppermute | solution.py:18
  86.4 5.0 %collective-permute-start.25 = (bf16[2,16,2048]{2,1,0:T(8,128)(2,1)S(1)}, bf16[2,16,2048]{2,1,0:T(8,128)(2,1)S(1)}, u32[]{:S(2)}, u32[]{:S(2)}) collective-permute-start(bf16[2,16,2048]{2,1,0:T(8,128)(2,1)S(1)} %fusion.18), channel_id=1, source_target_pairs={{0,2},{2,0},{4,6},{6,4},{8,10},{10,8},{12,14},{14,12},{1,3},{3,1},... | collective-permute-start | bytes 393224 | tf_op jit(solution)/shard_map/ppermute | solution.py:18
  91.5 5.2 %collective-permute-start.26 = (bf16[16,2048]{1,0:T(8,128)(2,1)S(1)}, bf16[16,2048]{1,0:T(8,128)(2,1)S(1)}, u32[]{:S(2)}, u32[]{:S(2)}) collective-permute-start(bf16[16,2048]{1,0:T(8,128)(2,1)S(1)} %fusion.22), channel_id=1, source_target_pairs={{0,8},{2,10},{4,12},{6,14},{8,0},{10,2},{12,4},{14,6},{1,9},{3,11}... | collective-permute-start | bytes 196616 | tf_op jit(solution)/shard_map/ppermute | solution.py:18

commit v21 on v15

--- a/solution.py
+++ b/solution.py
@@ -84,8 +84,9 @@
 def orders_of(axis):
     bits = list(range((lax.axis_size(axis) - 1).bit_length()))
     if len(bits) < 3:
-        return [bits, bits]
-    return [bits, [bits[1], bits[0]] + bits[2:]]
+        return [bits] * 4
+    heads = [(0, 1, 2), (1, 0, 2), (0, 2, 1), (1, 2, 0)]
+    return [list(head) + bits[3:] for head in heads]
 
 
 def fetch_tiles(slab_ref, buffer, arrived):
@@ -307,7 +308,7 @@
     step = cols_here // CHUNKS
     for c in range(CHUNKS):
         span = slice(c * step, (c + 1) * step)
-        shared = sum_and_share(local_cols[c], "row", orders[c % 2], 1.0 / root_rows)
+        shared = sum_and_share(local_cols[c], "row", orders[c % 4], 1.0 / root_rows)
         partial_sketch = partial_sketch + lax.dot_general(
             activations[:, span],
             shared,

time: 82.8 us -> 83.9 us (1.013)
  waiting for transfers between devices: 19.5 us -> 20.5 us
    ppermute x34, waiting for transfers between devices: 17 us -> 18 us  [swap(): return lax.ppermute(value, axis, [(i, i ^ distance) for i in range(size)])]
where the time goes in v21:
time: 83.9 us; the launch traced here: 83.7 us
  starting transfers between devices  49 us (58%)
  waiting for transfers between devices  20.5 us (24%)
  Pallas kernels  8.12 us (10%)
  other arithmetic  2.12 us (3%)
  matrix products  1.75 us (2%)
  between operations  1.11 us (1%)
  local copies, waits for them, and re-layouts  1.05 us (1%)
    ppermute x34, starting transfers between devices, swap(): return lax.ppermute(value, axis, [(i, i ^ distance) for i in range(size)])  43.9 us
    ppermute x34, waiting for transfers between devices, swap(): return lax.ppermute(value, axis, [(i, i ^ distance) for i in range(size)])  18 us
    ppermute x4, starting transfers between devices, row_sum(): terms.append(lax.ppermute(value, ('row', 'col'), pairs))  5.1 us
    pallas_call x1, Pallas kernels, make_basis(): pl.pallas_call(functools.partial(basis_kernel, total_cols, root_rows), ou...  4.63 us
    pallas_call x1, Pallas kernels, first_product(): pl.pallas_call(sketch_kernel, out_shape=[jax.ShapeDtypeStruct((width, col...  2.99 us
    ppermute x4, waiting for transfers between devices, row_sum(): terms.append(lax.ppermute(value, ('row', 'col'), pairs))  2.59 us
    dot_general x4, matrix products, per_device(): lax.dot_general(activations[:, span], shared, (((1,), (1,)), ((), ())), p...  1.75 us
  transfers between devices with their start and end apart: 38, of which 18 were waited for; matrix products, arithmetic and copies ran while one was open for 3% of the time, Pallas kernels for 0%

profile of v21, /device:TPU:0, one launch (start us, length us, event | category | flops | bytes accessed | tf_op | source)
XLA Modules:
  0.0 83.7 jit_solution(9486526216487899354)
XLA Ops:
  0.7 0.9 %copy-done = bf16[512,128]{1,0:T(8,128)(2,1)S(1)} copy-done((bf16[512,128]{1,0:T(8,128)(2,1)S(1)}, bf16[512,128]{1,0:T(8,128)(2,1)}, u32[]{:S(2)}) %copy-start) | copy-done | bytes 131096
  1.6 3.0 %first_product.1 = (f32[128,1024]{1,0:T(8,128)S(1)}, f32[128,1024]{1,0:T(8,128)S(1)}, f32[128,1024]{1,0:T(8,128)S(1)}, f32[128,1024]{1,0:T(8,128)S(1)}) custom-call(bf16[512,128]{1,0:T(8,128)(2,1)S(1)} %copy-done, bf16[512,4096]{1,0:T(8,128)(2,1)} %slab_ref.3), custom_call_target="tpu_custom_call" | custom-call | flops 536870912 | bytes 4194304 | tf_op jit(solution)/shard_map/first_product/pallas_call | solution.py:119
  4.6 3.1 %collective-permute-start.15 = (bf16[128,512]{1,0:T(8,128)(2,1)S(1)}, bf16[128,512]{1,0:T(8,128)(2,1)S(1)}, u32[]{:S(2)}, u32[]{:S(2)}) collective-permute-start(bf16[128,512]{1,0:T(8,128)(2,1)S(1)} %select_convert_fusion.4), channel_id=1, source_target_pairs={{0,4},{2,6},{4,0},{6,2},{8,12},{10,14},{12,8},{14,10},{1,5},{3,7},... | collective-permute-start | bytes 393224 | tf_op jit(solution)/shard_map/ppermute | solution.py:18
  7.7 1.6 %collective-permute-start.10 = (bf16[128,512]{1,0:T(8,128)(2,1)S(1)}, bf16[128,512]{1,0:T(8,128)(2,1)S(1)}, u32[]{:S(2)}, u32[]{:S(2)}) collective-permute-start(bf16[128,512]{1,0:T(8,128)(2,1)S(1)} %select_convert_fusion.5), channel_id=1, source_target_pairs={{0,2},{2,0},{4,6},{6,4},{8,10},{10,8},{12,14},{14,12},{1,3},{3,1},... | collective-permute-start | bytes 393224 | tf_op jit(solution)/shard_map/ppermute | solution.py:18
  10.0 1.6 %collective-permute-done.15 = bf16[128,512]{1,0:T(8,128)(2,1)S(1)} collective-permute-done((bf16[128,512]{1,0:T(8,128)(2,1)S(1)}, bf16[128,512]{1,0:T(8,128)(2,1)S(1)}, u32[]{:S(2)}, u32[]{:S(2)}) %collective-permute-start.15) | collective-permute-done | bytes 131104 | tf_op jit(solution)/shard_map/ppermute | solution.py:18
  11.7 2.7 %collective-permute-start.16 = (bf16[128,256]{1,0:T(8,128)(2,1)S(1)}, bf16[128,256]{1,0:T(8,128)(2,1)S(1)}, u32[]{:S(2)}, u32[]{:S(2)}) collective-permute-start(bf16[128,256]{1,0:T(8,128)(2,1)S(1)} %select_convert_fusion.12), channel_id=1, source_target_pairs={{0,8},{2,10},{4,12},{6,14},{8,0},{10,2},{12,4},{14,6},{1,9},{3,11}... | collective-permute-start | bytes 196616 | tf_op jit(solution)/shard_map/ppermute | solution.py:18
  14.4 2.3 %collective-permute-start.11 = (bf16[128,256]{1,0:T(8,128)(2,1)S(1)}, bf16[128,256]{1,0:T(8,128)(2,1)S(1)}, u32[]{:S(2)}, u32[]{:S(2)}) collective-permute-start(bf16[128,256]{1,0:T(8,128)(2,1)S(1)} %select_convert_fusion.13), channel_id=1, source_target_pairs={{0,8},{2,10},{4,12},{6,14},{8,0},{10,2},{12,4},{14,6},{1,9},{3,11}... | collective-permute-start | bytes 196616 | tf_op jit(solution)/shard_map/ppermute | solution.py:18
  16.8 1.7 %collective-permute-start.6 = (bf16[128,256]{1,0:T(8,128)(2,1)S(1)}, bf16[128,256]{1,0:T(8,128)(2,1)S(1)}, u32[]{:S(2)}, u32[]{:S(2)}) collective-permute-start(bf16[128,256]{1,0:T(8,128)(2,1)S(1)} %select_convert_fusion.14), channel_id=1, source_target_pairs={{0,2},{2,0},{4,6},{6,4},{8,10},{10,8},{12,14},{14,12},{1,3},{3,1},... | collective-permute-start | bytes 196616 | tf_op jit(solution)/shard_map/ppermute | solution.py:18
  19.1 1.8 %collective-permute-start.17 = (bf16[128,256]{1,0:T(8,128)(2,1)S(1)}, bf16[128,256]{1,0:T(8,128)(2,1)S(1)}, u32[]{:S(2)}, u32[]{:S(2)}) collective-permute-start(bf16[128,256]{1,0:T(8,128)(2,1)S(1)} %fusion.41), channel_id=1, source_target_pairs={{0,2},{2,0},{4,6},{6,4},{8,10},{10,8},{12,14},{14,12},{1,3},{3,1},... | collective-permute-start | bytes 196616 | tf_op jit(solution)/shard_map/ppermute | solution.py:18
  20.9 1.3 %collective-permute-start.12 = (bf16[128,256]{1,0:T(8,128)(2,1)S(1)}, bf16[128,256]{1,0:T(8,128)(2,1)S(1)}, u32[]{:S(2)}, u32[]{:S(2)}) collective-permute-start(bf16[128,256]{1,0:T(8,128)(2,1)S(1)} %fusion.40), channel_id=1, source_target_pairs={{0,4},{2,6},{4,0},{6,2},{8,12},{10,14},{12,8},{14,10},{1,5},{3,7},... | collective-permute-start | bytes 196616 | tf_op jit(solution)/shard_map/ppermute | solution.py:18
  22.2 2.0 %collective-permute-start.7 = (bf16[128,256]{1,0:T(8,128)(2,1)S(1)}, bf16[128,256]{1,0:T(8,128)(2,1)S(1)}, u32[]{:S(2)}, u32[]{:S(2)}) collective-permute-start(bf16[128,256]{1,0:T(8,128)(2,1)S(1)} %fusion.39), channel_id=1, source_target_pairs={{0,8},{2,10},{4,12},{6,14},{8,0},{10,2},{12,4},{14,6},{1,9},{3,11}... | collective-permute-start | bytes 196616 | tf_op jit(solution)/shard_map/ppermute | solution.py:18
  24.3 1.1 %collective-permute-start.2 = (bf16[128,256]{1,0:T(8,128)(2,1)S(1)}, bf16[128,256]{1,0:T(8,128)(2,1)S(1)}, u32[]{:S(2)}, u32[]{:S(2)}) collective-permute-start(bf16[128,256]{1,0:T(8,128)(2,1)S(1)} %fusion.38), channel_id=1, source_target_pairs={{0,8},{2,10},{4,12},{6,14},{8,0},{10,2},{12,4},{14,6},{1,9},{3,11}... | collective-permute-start | bytes 196616 | tf_op jit(solution)/shard_map/ppermute | solution.py:18
  25.4 2.0 %collective-permute-start.18 = (bf16[128,256]{1,0:T(8,128)(2,1)S(1)}, bf16[128,256]{1,0:T(8,128)(2,1)S(1)}, u32[]{:S(2)}, u32[]{:S(2)}) collective-permute-start(bf16[128,256]{1,0:T(8,128)(2,1)S(1)} %multiply_convert_fusion), channel_id=1, source_target_pairs={{0,8},{2,10},{4,12},{6,14},{8,0},{10,2},{12,4},{14,6},{1,9},{3,11}... | collective-permute-start | bytes 196616 | tf_op jit(solution)/shard_map/ppermute | solution.py:18
  27.4 1.1 %collective-permute-start.13 = (bf16[128,256]{1,0:T(8,128)(2,1)S(1)}, bf16[128,256]{1,0:T(8,128)(2,1)S(1)}, u32[]{:S(2)}, u32[]{:S(2)}) collective-permute-start(bf16[128,256]{1,0:T(8,128)(2,1)S(1)} %multiply_convert_fusion.1), channel_id=1, source_target_pairs={{0,8},{2,10},{4,12},{6,14},{8,0},{10,2},{12,4},{14,6},{1,9},{3,11}... | collective-permute-start | bytes 196616 | tf_op jit(solution)/shard_map/ppermute | solution.py:18
  28.5 4.0 %collective-permute-done.7 = bf16[128,256]{1,0:T(8,128)(2,1)S(1)} collective-permute-done((bf16[128,256]{1,0:T(8,128)(2,1)S(1)}, bf16[128,256]{1,0:T(8,128)(2,1)S(1)}, u32[]{:S(2)}, u32[]{:S(2)}) %collective-permute-start.7) | collective-permute-done | bytes 65568 | tf_op jit(solution)/shard_map/ppermute | solution.py:18
  32.5 0.9 %collective-permute-done.2 = bf16[128,256]{1,0:T(8,128)(2,1)S(1)} collective-permute-done((bf16[128,256]{1,0:T(8,128)(2,1)S(1)}, bf16[128,256]{1,0:T(8,128)(2,1)S(1)}, u32[]{:S(2)}, u32[]{:S(2)}) %collective-permute-start.2) | collective-permute-done | bytes 65568 | tf_op jit(solution)/shard_map/ppermute | solution.py:18
  33.5 0.6 collective-permute-done.18
  34.2 1.4 %collective-permute-start.19 = (bf16[128,512]{1,0:T(8,128)(2,1)S(1)}, bf16[128,512]{1,0:T(8,128)(2,1)S(1)}, u32[]{:S(2)}, u32[]{:S(2)}) collective-permute-start(bf16[128,512]{1,0:T(8,128)(2,1)S(1)} %pad_maximum_fusion.4), channel_id=1, source_target_pairs={{0,4},{2,6},{4,0},{6,2},{8,12},{10,14},{12,8},{14,10},{1,5},{3,7},... | collective-permute-start | bytes 393224 | tf_op jit(solution)/shard_map/ppermute | solution.py:18
  35.7 1.2 %collective-permute-start.14 = (bf16[128,512]{1,0:T(8,128)(2,1)S(1)}, bf16[128,512]{1,0:T(8,128)(2,1)S(1)}, u32[]{:S(2)}, u32[]{:S(2)}) collective-permute-start(bf16[128,512]{1,0:T(8,128)(2,1)S(1)} %pad_maximum_fusion.3), channel_id=1, source_target_pairs={{0,2},{2,0},{4,6},{6,4},{8,10},{10,8},{12,14},{14,12},{1,3},{3,1},... | collective-permute-start | bytes 393224 | tf_op jit(solution)/shard_map/ppermute | solution.py:18
  37.5 0.7 collective-permute-done.3
  38.3 1.4 %collective-permute-start.4 = (bf16[128,512]{1,0:T(8,128)(2,1)S(1)}, bf16[128,512]{1,0:T(8,128)(2,1)S(1)}, u32[]{:S(2)}, u32[]{:S(2)}) collective-permute-start(bf16[128,512]{1,0:T(8,128)(2,1)S(1)} %pad_maximum_fusion.1), channel_id=1, source_target_pairs={{0,2},{2,0},{4,6},{6,4},{8,10},{10,8},{12,14},{14,12},{1,3},{3,1},... | collective-permute-start | bytes 393224 | tf_op jit(solution)/shard_map/ppermute | solution.py:18
  41.2 1.3 %collective-permute-done.9 = bf16[128,512]{1,0:T(8,128)(2,1)S(1)} collective-permute-done((bf16[128,512]{1,0:T(8,128)(2,1)S(1)}, bf16[128,512]{1,0:T(8,128)(2,1)S(1)}, u32[]{:S(2)}, u32[]{:S(2)}) %collective-permute-start.9) | collective-permute-done | bytes 131104 | tf_op jit(solution)/shard_map/ppermute | solution.py:18
  43.9 1.5 %collective-permute-done.20.other_ref = f32[512,128]{1,0:T(8,128)S(1)} collective-permute-done((f32[512,128]{1,0:T(8,128)S(1)}, f32[512,128]{1,0:T(8,128)S(1)}, u32[]{:S(2)}, u32[]{:S(2)}) %collective-permute-start.20) | collective-permute-done | bytes 262176 | tf_op jit(solution)/shard_map/ppermute | solution.py:18
  45.9 1.7 %collective-permute-start.24 = (f32[72,128]{1,0:T(8,128)S(1)}, f32[72,128]{1,0:T(8,128)S(1)}, u32[]{:S(2)}, u32[]{:S(2)}) collective-permute-start(f32[72,128]{1,0:T(8,128)S(1)} %make_gram.1), channel_id=1, source_target_pairs={{0,10},{1,15},{2,8},{3,13},{4,14},{5,11},{6,12},{7,9},{8,2},{9,7},... | collective-permute-start | bytes 110600 | tf_op jit(solution)/shard_map/ppermute | solution.py:36
  47.7 2.0 %collective-permute-start.23 = (f32[72,128]{1,0:T(8,128)S(1)}, f32[72,128]{1,0:T(8,128)S(1)}, u32[]{:S(2)}, u32[]{:S(2)}) collective-permute-start(f32[72,128]{1,0:T(8,128)S(1)} %make_gram.1), channel_id=1, source_target_pairs={{0,8},{1,13},{2,10},{3,15},{4,12},{5,9},{6,14},{7,11},{8,0},{9,5},... | collective-permute-start | bytes 110600 | tf_op jit(solution)/shard_map/ppermute | solution.py:36
  49.7 0.7 collective-permute-start.22
  50.4 0.7 collective-permute-start.21
  51.0 1.5 %collective-permute-done.24 = f32[72,128]{1,0:T(8,128)S(1)} collective-permute-done((f32[72,128]{1,0:T(8,128)S(1)}, f32[72,128]{1,0:T(8,128)S(1)}, u32[]{:S(2)}, u32[]{:S(2)}) %collective-permute-start.24) | collective-permute-done | bytes 36896 | tf_op jit(solution)/shard_map/ppermute | solution.py:36
  52.5 0.9 %collective-permute-done.23 = f32[72,128]{1,0:T(8,128)S(1)} collective-permute-done((f32[72,128]{1,0:T(8,128)S(1)}, f32[72,128]{1,0:T(8,128)S(1)}, u32[]{:S(2)}, u32[]{:S(2)}) %collective-permute-start.23) | collective-permute-done | bytes 36896 | tf_op jit(solution)/shard_map/ppermute | solution.py:36
  53.7 1.4 %collective-permute-start.25 = (f32[72,128]{1,0:T(8,128)S(1)}, f32[72,128]{1,0:T(8,128)S(1)}, u32[]{:S(2)}, u32[]{:S(2)}) collective-permute-start(f32[72,128]{1,0:T(8,128)S(1)} %add_add_fusion), channel_id=1, source_target_pairs={{0,1},{1,0},{2,3},{3,2},{4,5},{5,4},{6,7},{7,6},{8,9},{9,8},{10,11... | collective-permute-start | bytes 110600 | tf_op jit(solution)/shard_map/ppermute | solution.py:18
  55.1 0.9 %collective-permute-done.25 = f32[72,128]{1,0:T(8,128)S(1)} collective-permute-done((f32[72,128]{1,0:T(8,128)S(1)}, f32[72,128]{1,0:T(8,128)S(1)}, u32[]{:S(2)}, u32[]{:S(2)}) %collective-permute-start.25) | collective-permute-done | bytes 36896 | tf_op jit(solution)/shard_map/ppermute | solution.py:18
  56.0 4.6 %make_basis.1 = (f32[512,128]{1,0:T(8,128)}, f32[128,1024]{1,0:T(8,128)S(1)}, f32[128,1024]{1,0:T(8,128)S(1)}, f32[128,1024]{1,0:T(8,128)S(1)}, f32[128,1024]{1,0:T(8,128)S(1)}) custom-call(f32[72,128]{1,0:T(8,128)S(1)} %add.116.gram_ref, f32[512,128]{1,0:T(8,128)S(1)} %fusion.2.mine_ref, f32[512,128]{1,0:T(8,128)S(1)} %collective-permute-done.20.other_ref, ...), custom_call_target="tpu_custom_call" | custom-call | tf_op jit(solution)/shard_map/make_basis/pallas_call | solution.py:279
  60.7 1.4 %collective-permute-start.26 = (bf16[2,2,16,1024]{3,2,0,1:T(8,128)(2,1)S(1)}, bf16[2,2,16,1024]{3,2,0,1:T(8,128)(2,1)S(1)}, u32[]{:S(2)}, u32[]{:S(2)}) collective-permute-start(bf16[2,2,16,1024]{3,2,0,1:T(8,128)(2,1)S(1)} %fusion.22), channel_id=1, source_target_pairs={{0,2},{2,0},{4,6},{6,4},{8,10},{10,8},{12,14},{14,12},{1,3},{3,1},... | collective-permute-start | bytes 393224 | tf_op jit(solution)/shard_map/ppermute | solution.py:18
  62.1 1.8 %collective-permute-start.29 = (bf16[2,2,16,1024]{3,2,0,1:T(8,128)(2,1)S(1)}, bf16[2,2,16,1024]{3,2,0,1:T(8,128)(2,1)S(1)}, u32[]{:S(2)}, u32[]{:S(2)}) collective-permute-start(bf16[2,2,16,1024]{3,2,0,1:T(8,128)(2,1)S(1)} %fusion.23), channel_id=1, source_target_pairs={{0,4},{2,6},{4,0},{6,2},{8,12},{10,14},{12,8},{14,10},{1,5},{3,7},... | collective-permute-start | bytes 393224 | tf_op jit(solution)/shard_map/ppermute | solution.py:18
  64.0 0.8 collective-permute-start.32
  65.2 1.3 %collective-permute-done.26 = bf16[2,2,16,1024]{3,2,0,1:T(8,128)(2,1)S(1)} collective-permute-done((bf16[2,2,16,1024]{3,2,0,1:T(8,128)(2,1)S(1)}, bf16[2,2,16,1024]{3,2,0,1:T(8,128)(2,1)S(1)}, u32[]{:S(2)}, u32[]{:S(2)}) %collective-permute-start.26) | collective-permute-done | bytes 131104 | tf_op jit(solution)/shard_map/ppermute | solution.py:18
  66.6 2.4 %collective-permute-start.27 = (bf16[2,16,1024]{2,1,0:T(8,128)(2,1)S(1)}, bf16[2,16,1024]{2,1,0:T(8,128)(2,1)S(1)}, u32[]{:S(2)}, u32[]{:S(2)}) collective-permute-start(bf16[2,16,1024]{2,1,0:T(8,128)(2,1)S(1)} %fusion.26), channel_id=1, source_target_pairs={{0,4},{2,6},{4,0},{6,2},{8,12},{10,14},{12,8},{14,10},{1,5},{3,7},... | collective-permute-start | bytes 196616 | tf_op jit(solution)/shard_map/ppermute | solution.py:18
  69.0 1.4 %collective-permute-start.30 = (bf16[2,16,1024]{2,1,0:T(8,128)(2,1)S(1)}, bf16[2,16,1024]{2,1,0:T(8,128)(2,1)S(1)}, u32[]{:S(2)}, u32[]{:S(2)}) collective-permute-start(bf16[2,16,1024]{2,1,0:T(8,128)(2,1)S(1)} %fusion.27), channel_id=1, source_target_pairs={{0,2},{2,0},{4,6},{6,4},{8,10},{10,8},{12,14},{14,12},{1,3},{3,1},... | collective-permute-start | bytes 196616 | tf_op jit(solution)/shard_map/ppermute | solution.py:18
  70.5 0.8 collective-permute-start.33
  71.3 1.5 %collective-permute-start.36 = (bf16[2,16,1024]{2,1,0:T(8,128)(2,1)S(1)}, bf16[2,16,1024]{2,1,0:T(8,128)(2,1)S(1)}, u32[]{:S(2)}, u32[]{:S(2)}) collective-permute-start(bf16[2,16,1024]{2,1,0:T(8,128)(2,1)S(1)} %fusion.29), channel_id=1, source_target_pairs={{0,2},{2,0},{4,6},{6,4},{8,10},{10,8},{12,14},{14,12},{1,3},{3,1},... | collective-permute-start | bytes 196616 | tf_op jit(solution)/shard_map/ppermute | solution.py:18
  72.9 1.7 %collective-permute-start.28 = (bf16[16,1024]{1,0:T(8,128)(2,1)S(1)}, bf16[16,1024]{1,0:T(8,128)(2,1)S(1)}, u32[]{:S(2)}, u32[]{:S(2)}) collective-permute-start(bf16[16,1024]{1,0:T(8,128)(2,1)S(1)} %fusion.34), channel_id=1, source_target_pairs={{0,8},{2,10},{4,12},{6,14},{8,0},{10,2},{12,4},{14,6},{1,9},{3,11}... | collective-permute-start | bytes 98312 | tf_op jit(solution)/shard_map/ppermute | solution.py:18
  74.6 1.4 %collective-permute-start.31 = (bf16[16,1024]{1,0:T(8,128)(2,1)S(1)}, bf16[16,1024]{1,0:T(8,128)(2,1)S(1)}, u32[]{:S(2)}, u32[]{:S(2)}) collective-permute-start(bf16[16,1024]{1,0:T(8,128)(2,1)S(1)} %fusion.35), channel_id=1, source_target_pairs={{0,8},{2,10},{4,12},{6,14},{8,0},{10,2},{12,4},{14,6},{1,9},{3,11}... | collective-permute-start | bytes 98312 | tf_op jit(solution)/shard_map/ppermute | solution.py:18
  76.0 1.7 %collective-permute-start.34 = (bf16[16,1024]{1,0:T(8,128)(2,1)S(1)}, bf16[16,1024]{1,0:T(8,128)(2,1)S(1)}, u32[]{:S(2)}, u32[]{:S(2)}) collective-permute-start(bf16[16,1024]{1,0:T(8,128)(2,1)S(1)} %fusion.36), channel_id=1, source_target_pairs={{0,8},{2,10},{4,12},{6,14},{8,0},{10,2},{12,4},{14,6},{1,9},{3,11}... | collective-permute-start | bytes 98312 | tf_op jit(solution)/shard_map/ppermute | solution.py:18
  77.8 1.4 %collective-permute-start.37 = (bf16[16,1024]{1,0:T(8,128)(2,1)S(1)}, bf16[16,1024]{1,0:T(8,128)(2,1)S(1)}, u32[]{:S(2)}, u32[]{:S(2)}) collective-permute-start(bf16[16,1024]{1,0:T(8,128)(2,1)S(1)} %fusion.37), channel_id=1, source_target_pairs={{0,8},{2,10},{4,12},{6,14},{8,0},{10,2},{12,4},{14,6},{1,9},{3,11}... | collective-permute-start | bytes 98312 | tf_op jit(solution)/shard_map/ppermute | solution.py:18
  79.2 1.1 %collective-permute-done.31 = bf16[16,1024]{1,0:T(8,128)(2,1)S(1)} collective-permute-done((bf16[16,1024]{1,0:T(8,128)(2,1)S(1)}, bf16[16,1024]{1,0:T(8,128)(2,1)S(1)}, u32[]{:S(2)}, u32[]{:S(2)}) %collective-permute-start.31) | collective-permute-done | bytes 32800 | tf_op jit(solution)/shard_map/ppermute | solution.py:18
  80.3 0.6 collective-permute-done.34
  80.9 2.1 %collective-permute-done.37 = bf16[16,1024]{1,0:T(8,128)(2,1)S(1)} collective-permute-done((bf16[16,1024]{1,0:T(8,128)(2,1)S(1)}, bf16[16,1024]{1,0:T(8,128)(2,1)S(1)}, u32[]{:S(2)}, u32[]{:S(2)}) %collective-permute-start.37) | collective-permute-done | bytes 32800 | tf_op jit(solution)/shard_map/ppermute | solution.py:18
  83.0 0.7 pad_maximum_fusion
  (102 shorter events, 7.2 us)
Async XLA Ops:
  0.6 0.9 %copy-start = (bf16[512,128]{1,0:T(8,128)(2,1)S(1)}, bf16[512,128]{1,0:T(8,128)(2,1)}, u32[]{:S(2)}) copy-start(bf16[512,128]{1,0:T(8,128)(2,1)} %start_ref.1) | copy-start | bytes 393220
  4.6 7.0 %collective-permute-start.15 = (bf16[128,512]{1,0:T(8,128)(2,1)S(1)}, bf16[128,512]{1,0:T(8,128)(2,1)S(1)}, u32[]{:S(2)}, u32[]{:S(2)}) collective-permute-start(bf16[128,512]{1,0:T(8,128)(2,1)S(1)} %select_convert_fusion.4), channel_id=1, source_target_pairs={{0,4},{2,6},{4,0},{6,2},{8,12},{10,14},{12,8},{14,10},{1,5},{3,7},... | collective-permute-start | bytes 393224 | tf_op jit(solution)/shard_map/ppermute | solution.py:18
  7.7 6.6 %collective-permute-start.10 = (bf16[128,512]{1,0:T(8,128)(2,1)S(1)}, bf16[128,512]{1,0:T(8,128)(2,1)S(1)}, u32[]{:S(2)}, u32[]{:S(2)}) collective-permute-start(bf16[128,512]{1,0:T(8,128)(2,1)S(1)} %select_convert_fusion.5), channel_id=1, source_target_pairs={{0,2},{2,0},{4,6},{6,4},{8,10},{10,8},{12,14},{14,12},{1,3},{3,1},... | collective-permute-start | bytes 393224 | tf_op jit(solution)/shard_map/ppermute | solution.py:18
  9.3 7.4 %collective-permute-start.5 = (bf16[128,512]{1,0:T(8,128)(2,1)S(1)}, bf16[128,512]{1,0:T(8,128)(2,1)S(1)}, u32[]{:S(2)}, u32[]{:S(2)}) collective-permute-start(bf16[128,512]{1,0:T(8,128)(2,1)S(1)} %select_convert_fusion.6), channel_id=1, source_target_pairs={{0,4},{2,6},{4,0},{6,2},{8,12},{10,14},{12,8},{14,10},{1,5},{3,7},... | collective-permute-start | bytes 393224 | tf_op jit(solution)/shard_map/ppermute | solution.py:18
  9.8 8.7 %collective-permute-start = (bf16[128,512]{1,0:T(8,128)(2,1)S(1)}, bf16[128,512]{1,0:T(8,128)(2,1)S(1)}, u32[]{:S(2)}, u32[]{:S(2)}) collective-permute-start(bf16[128,512]{1,0:T(8,128)(2,1)S(1)} %select_convert_fusion.7), channel_id=1, source_target_pairs={{0,2},{2,0},{4,6},{6,4},{8,10},{10,8},{12,14},{14,12},{1,3},{3,1},... | collective-permute-start | bytes 393224 | tf_op jit(solution)/shard_map/ppermute | solution.py:18
  11.7 7.4 %collective-permute-start.16 = (bf16[128,256]{1,0:T(8,128)(2,1)S(1)}, bf16[128,256]{1,0:T(8,128)(2,1)S(1)}, u32[]{:S(2)}, u32[]{:S(2)}) collective-permute-start(bf16[128,256]{1,0:T(8,128)(2,1)S(1)} %select_convert_fusion.12), channel_id=1, source_target_pairs={{0,8},{2,10},{4,12},{6,14},{8,0},{10,2},{12,4},{14,6},{1,9},{3,11}... | collective-permute-start | bytes 196616 | tf_op jit(solution)/shard_map/ppermute | solution.py:18
  14.4 25.4 %copy-start.1 = (bf16[512,4096]{1,0:T(8,128)(2,1)S(1)}, bf16[512,4096]{1,0:T(8,128)(2,1)}, u32[]{:S(2)}) copy-start(bf16[512,4096]{1,0:T(8,128)(2,1)} %slab_ref.3) | copy-start | bytes 12582916
  14.4 6.4 %collective-permute-start.11 = (bf16[128,256]{1,0:T(8,128)(2,1)S(1)}, bf16[128,256]{1,0:T(8,128)(2,1)S(1)}, u32[]{:S(2)}, u32[]{:S(2)}) collective-permute-start(bf16[128,256]{1,0:T(8,128)(2,1)S(1)} %select_convert_fusion.13), channel_id=1, source_target_pairs={{0,8},{2,10},{4,12},{6,14},{8,0},{10,2},{12,4},{14,6},{1,9},{3,11}... | collective-permute-start | bytes 196616 | tf_op jit(solution)/shard_map/ppermute | solution.py:18
  16.8 5.4 %collective-permute-start.6 = (bf16[128,256]{1,0:T(8,128)(2,1)S(1)}, bf16[128,256]{1,0:T(8,128)(2,1)S(1)}, u32[]{:S(2)}, u32[]{:S(2)}) collective-permute-start(bf16[128,256]{1,0:T(8,128)(2,1)S(1)} %select_convert_fusion.14), channel_id=1, source_target_pairs={{0,2},{2,0},{4,6},{6,4},{8,10},{10,8},{12,14},{14,12},{1,3},{3,1},... | collective-permute-start | bytes 196616 | tf_op jit(solution)/shard_map/ppermute | solution.py:18
  18.6 5.6 %collective-permute-start.1 = (bf16[128,256]{1,0:T(8,128)(2,1)S(1)}, bf16[128,256]{1,0:T(8,128)(2,1)S(1)}, u32[]{:S(2)}, u32[]{:S(2)}) collective-permute-start(bf16[128,256]{1,0:T(8,128)(2,1)S(1)} %select_convert_fusion.15), channel_id=1, source_target_pairs={{0,4},{2,6},{4,0},{6,2},{8,12},{10,14},{12,8},{14,10},{1,5},{3,7},... | collective-permute-start | bytes 196616 | tf_op jit(solution)/shard_map/ppermute | solution.py:18
  19.1 6.2 %collective-permute-start.17 = (bf16[128,256]{1,0:T(8,128)(2,1)S(1)}, bf16[128,256]{1,0:T(8,128)(2,1)S(1)}, u32[]{:S(2)}, u32[]{:S(2)}) collective-permute-start(bf16[128,256]{1,0:T(8,128)(2,1)S(1)} %fusion.41), channel_id=1, source_target_pairs={{0,2},{2,0},{4,6},{6,4},{8,10},{10,8},{12,14},{14,12},{1,3},{3,1},... | collective-permute-start | bytes 196616 | tf_op jit(solution)/shard_map/ppermute | solution.py:18
  20.9 6.5 %collective-permute-start.12 = (bf16[128,256]{1,0:T(8,128)(2,1)S(1)}, bf16[128,256]{1,0:T(8,128)(2,1)S(1)}, u32[]{:S(2)}, u32[]{:S(2)}) collective-permute-start(bf16[128,256]{1,0:T(8,128)(2,1)S(1)} %fusion.40), channel_id=1, source_target_pairs={{0,4},{2,6},{4,0},{6,2},{8,12},{10,14},{12,8},{14,10},{1,5},{3,7},... | collective-permute-start | bytes 196616 | tf_op jit(solution)/shard_map/ppermute | solution.py:18
  22.2 10.2 %collective-permute-start.7 = (bf16[128,256]{1,0:T(8,128)(2,1)S(1)}, bf16[128,256]{1,0:T(8,128)(2,1)S(1)}, u32[]{:S(2)}, u32[]{:S(2)}) collective-permute-start(bf16[128,256]{1,0:T(8,128)(2,1)S(1)} %fusion.39), channel_id=1, source_target_pairs={{0,8},{2,10},{4,12},{6,14},{8,0},{10,2},{12,4},{14,6},{1,9},{3,11}... | collective-permute-start | bytes 196616 | tf_op jit(solution)/shard_map/ppermute | solution.py:18
  24.3 9.1 %collective-permute-start.2 = (bf16[128,256]{1,0:T(8,128)(2,1)S(1)}, bf16[128,256]{1,0:T(8,128)(2,1)S(1)}, u32[]{:S(2)}, u32[]{:S(2)}) collective-permute-start(bf16[128,256]{1,0:T(8,128)(2,1)S(1)} %fusion.38), channel_id=1, source_target_pairs={{0,8},{2,10},{4,12},{6,14},{8,0},{10,2},{12,4},{14,6},{1,9},{3,11}... | collective-permute-start | bytes 196616 | tf_op jit(solution)/shard_map/ppermute | solution.py:18
  25.4 8.8 %collective-permute-start.18 = (bf16[128,256]{1,0:T(8,128)(2,1)S(1)}, bf16[128,256]{1,0:T(8,128)(2,1)S(1)}, u32[]{:S(2)}, u32[]{:S(2)}) collective-permute-start(bf16[128,256]{1,0:T(8,128)(2,1)S(1)} %multiply_convert_fusion), channel_id=1, source_target_pairs={{0,8},{2,10},{4,12},{6,14},{8,0},{10,2},{12,4},{14,6},{1,9},{3,11}... | collective-permute-start | bytes 196616 | tf_op jit(solution)/shard_map/ppermute | solution.py:18
  27.4 8.2 %collective-permute-start.13 = (bf16[128,256]{1,0:T(8,128)(2,1)S(1)}, bf16[128,256]{1,0:T(8,128)(2,1)S(1)}, u32[]{:S(2)}, u32[]{:S(2)}) collective-permute-start(bf16[128,256]{1,0:T(8,128)(2,1)S(1)} %multiply_convert_fusion.1), channel_id=1, source_target_pairs={{0,8},{2,10},{4,12},{6,14},{8,0},{10,2},{12,4},{14,6},{1,9},{3,11}... | collective-permute-start | bytes 196616 | tf_op jit(solution)/shard_map/ppermute | solution.py:18
  32.5 4.9 %collective-permute-start.8 = (bf16[128,256]{1,0:T(8,128)(2,1)S(1)}, bf16[128,256]{1,0:T(8,128)(2,1)S(1)}, u32[]{:S(2)}, u32[]{:S(2)}) collective-permute-start(bf16[128,256]{1,0:T(8,128)(2,1)S(1)} %multiply_convert_fusion.2), channel_id=1, source_target_pairs={{0,2},{2,0},{4,6},{6,4},{8,10},{10,8},{12,14},{14,12},{1,3},{3,1},... | collective-permute-start | bytes 196616 | tf_op jit(solution)/shard_map/ppermute | solution.py:18
  33.4 4.8 %collective-permute-start.3 = (bf16[128,256]{1,0:T(8,128)(2,1)S(1)}, bf16[128,256]{1,0:T(8,128)(2,1)S(1)}, u32[]{:S(2)}, u32[]{:S(2)}) collective-permute-start(bf16[128,256]{1,0:T(8,128)(2,1)S(1)} %multiply_convert_fusion.3), channel_id=1, source_target_pairs={{0,4},{2,6},{4,0},{6,2},{8,12},{10,14},{12,8},{14,10},{1,5},{3,7},... | collective-permute-start | bytes 196616 | tf_op jit(solution)/shard_map/ppermute | solution.py:18
  34.2 5.5 %collective-permute-start.19 = (bf16[128,512]{1,0:T(8,128)(2,1)S(1)}, bf16[128,512]{1,0:T(8,128)(2,1)S(1)}, u32[]{:S(2)}, u32[]{:S(2)}) collective-permute-start(bf16[128,512]{1,0:T(8,128)(2,1)S(1)} %pad_maximum_fusion.4), channel_id=1, source_target_pairs={{0,4},{2,6},{4,0},{6,2},{8,12},{10,14},{12,8},{14,10},{1,5},{3,7},... | collective-permute-start | bytes 393224 | tf_op jit(solution)/shard_map/ppermute | solution.py:18
  35.7 5.0 %collective-permute-start.14 = (bf16[128,512]{1,0:T(8,128)(2,1)S(1)}, bf16[128,512]{1,0:T(8,128)(2,1)S(1)}, u32[]{:S(2)}, u32[]{:S(2)}) collective-permute-start(bf16[128,512]{1,0:T(8,128)(2,1)S(1)} %pad_maximum_fusion.3), channel_id=1, source_target_pairs={{0,2},{2,0},{4,6},{6,4},{8,10},{10,8},{12,14},{14,12},{1,3},{3,1},... | collective-permute-start | bytes 393224 | tf_op jit(solution)/shard_map/ppermute | solution.py:18
  37.5 5.0 %collective-permute-start.9 = (bf16[128,512]{1,0:T(8,128)(2,1)S(1)}, bf16[128,512]{1,0:T(8,128)(2,1)S(1)}, u32[]{:S(2)}, u32[]{:S(2)}) collective-permute-start(bf16[128,512]{1,0:T(8,128)(2,1)S(1)} %pad_maximum_fusion.2), channel_id=1, source_target_pairs={{0,4},{2,6},{4,0},{6,2},{8,12},{10,14},{12,8},{14,10},{1,5},{3,7},... | collective-permute-start | bytes 393224 | tf_op jit(solution)/shard_map/ppermute | solution.py:18
  38.3 5.0 %collective-permute-start.4 = (bf16[128,512]{1,0:T(8,128)(2,1)S(1)}, bf16[128,512]{1,0:T(8,128)(2,1)S(1)}, u32[]{:S(2)}, u32[]{:S(2)}) collective-permute-start(bf16[128,512]{1,0:T(8,128)(2,1)S(1)} %pad_maximum_fusion.1), channel_id=1, source_target_pairs={{0,2},{2,0},{4,6},{6,4},{8,10},{10,8},{12,14},{14,12},{1,3},{3,1},... | collective-permute-start | bytes 393224 | tf_op jit(solution)/shard_map/ppermute | solution.py:18
  43.8 1.6 %collective-permute-start.20 = (f32[512,128]{1,0:T(8,128)S(1)}, f32[512,128]{1,0:T(8,128)S(1)}, u32[]{:S(2)}, u32[]{:S(2)}) collective-permute-start(f32[512,128]{1,0:T(8,128)S(1)} %fusion.2.mine_ref), channel_id=1, source_target_pairs={{0,1},{1,0},{2,3},{3,2},{4,5},{5,4},{6,7},{7,6},{8,9},{9,8},{10,11... | collective-permute-start | bytes 786440 | tf_op jit(solution)/shard_map/ppermute | solution.py:18
  45.9 6.6 %collective-permute-start.24 = (f32[72,128]{1,0:T(8,128)S(1)}, f32[72,128]{1,0:T(8,128)S(1)}, u32[]{:S(2)}, u32[]{:S(2)}) collective-permute-start(f32[72,128]{1,0:T(8,128)S(1)} %make_gram.1), channel_id=1, source_target_pairs={{0,10},{1,15},{2,8},{3,13},{4,14},{5,11},{6,12},{7,9},{8,2},{9,7},... | collective-permute-start | bytes 110600 | tf_op jit(solution)/shard_map/ppermute | solution.py:36
  47.7 5.8 %collective-permute-start.23 = (f32[72,128]{1,0:T(8,128)S(1)}, f32[72,128]{1,0:T(8,128)S(1)}, u32[]{:S(2)}, u32[]{:S(2)}) collective-permute-start(f32[72,128]{1,0:T(8,128)S(1)} %make_gram.1), channel_id=1, source_target_pairs={{0,8},{1,13},{2,10},{3,15},{4,12},{5,9},{6,14},{7,11},{8,0},{9,5},... | collective-permute-start | bytes 110600 | tf_op jit(solution)/shard_map/ppermute | solution.py:36
  49.7 4.0 %collective-permute-start.22 = (f32[72,128]{1,0:T(8,128)S(1)}, f32[72,128]{1,0:T(8,128)S(1)}, u32[]{:S(2)}, u32[]{:S(2)}) collective-permute-start(f32[72,128]{1,0:T(8,128)S(1)} %make_gram.1), channel_id=1, source_target_pairs={{0,2},{1,7},{2,0},{3,5},{4,6},{5,3},{6,4},{7,1},{8,10},{9,15},{10,... | collective-permute-start | bytes 110600 | tf_op jit(solution)/shard_map/ppermute | solution.py:36
  50.4 3.3 %collective-permute-start.21 = (f32[72,128]{1,0:T(8,128)S(1)}, f32[72,128]{1,0:T(8,128)S(1)}, u32[]{:S(2)}, u32[]{:S(2)}) collective-permute-start(f32[72,128]{1,0:T(8,128)S(1)} %make_gram.1), channel_id=1, source_target_pairs={{1,5},{3,7},{5,1},{7,3},{9,13},{11,15},{13,9},{15,11},{17,21},{19,... | collective-permute-start | bytes 110600 | tf_op jit(solution)/shard_map/ppermute | solution.py:36
  53.7 2.3 %collective-permute-start.25 = (f32[72,128]{1,0:T(8,128)S(1)}, f32[72,128]{1,0:T(8,128)S(1)}, u32[]{:S(2)}, u32[]{:S(2)}) collective-permute-start(f32[72,128]{1,0:T(8,128)S(1)} %add_add_fusion), channel_id=1, source_target_pairs={{0,1},{1,0},{2,3},{3,2},{4,5},{5,4},{6,7},{7,6},{8,9},{9,8},{10,11... | collective-permute-start | bytes 110600 | tf_op jit(solution)/shard_map/ppermute | solution.py:18
  60.7 5.8 %collective-permute-start.26 = (bf16[2,2,16,1024]{3,2,0,1:T(8,128)(2,1)S(1)}, bf16[2,2,16,1024]{3,2,0,1:T(8,128)(2,1)S(1)}, u32[]{:S(2)}, u32[]{:S(2)}) collective-permute-start(bf16[2,2,16,1024]{3,2,0,1:T(8,128)(2,1)S(1)} %fusion.22), channel_id=1, source_target_pairs={{0,2},{2,0},{4,6},{6,4},{8,10},{10,8},{12,14},{14,12},{1,3},{3,1},... | collective-permute-start | bytes 393224 | tf_op jit(solution)/shard_map/ppermute | solution.py:18
  62.1 6.8 %collective-permute-start.29 = (bf16[2,2,16,1024]{3,2,0,1:T(8,128)(2,1)S(1)}, bf16[2,2,16,1024]{3,2,0,1:T(8,128)(2,1)S(1)}, u32[]{:S(2)}, u32[]{:S(2)}) collective-permute-start(bf16[2,2,16,1024]{3,2,0,1:T(8,128)(2,1)S(1)} %fusion.23), channel_id=1, source_target_pairs={{0,4},{2,6},{4,0},{6,2},{8,12},{10,14},{12,8},{14,10},{1,5},{3,7},... | collective-permute-start | bytes 393224 | tf_op jit(solution)/shard_map/ppermute | solution.py:18
  64.0 6.4 %collective-permute-start.32 = (bf16[2,2,16,1024]{3,2,0,1:T(8,128)(2,1)S(1)}, bf16[2,2,16,1024]{3,2,0,1:T(8,128)(2,1)S(1)}, u32[]{:S(2)}, u32[]{:S(2)}) collective-permute-start(bf16[2,2,16,1024]{3,2,0,1:T(8,128)(2,1)S(1)} %fusion.24), channel_id=1, source_target_pairs={{0,2},{2,0},{4,6},{6,4},{8,10},{10,8},{12,14},{14,12},{1,3},{3,1},... | collective-permute-start | bytes 393224 | tf_op jit(solution)/shard_map/ppermute | solution.py:18
  64.9 6.4 %collective-permute-start.35 = (bf16[2,2,16,1024]{3,2,0,1:T(8,128)(2,1)S(1)}, bf16[2,2,16,1024]{3,2,0,1:T(8,128)(2,1)S(1)}, u32[]{:S(2)}, u32[]{:S(2)}) collective-permute-start(bf16[2,2,16,1024]{3,2,0,1:T(8,128)(2,1)S(1)} %fusion.25), channel_id=1, source_target_pairs={{0,4},{2,6},{4,0},{6,2},{8,12},{10,14},{12,8},{14,10},{1,5},{3,7},... | collective-permute-start | bytes 393224 | tf_op jit(solution)/shard_map/ppermute | solution.py:18
  66.6 6.3 %collective-permute-start.27 = (bf16[2,16,1024]{2,1,0:T(8,128)(2,1)S(1)}, bf16[2,16,1024]{2,1,0:T(8,128)(2,1)S(1)}, u32[]{:S(2)}, u32[]{:S(2)}) collective-permute-start(bf16[2,16,1024]{2,1,0:T(8,128)(2,1)S(1)} %fusion.26), channel_id=1, source_target_pairs={{0,4},{2,6},{4,0},{6,2},{8,12},{10,14},{12,8},{14,10},{1,5},{3,7},... | collective-permute-start | bytes 196616 | tf_op jit(solution)/shard_map/ppermute | solution.py:18
  69.0 5.6 %collective-permute-start.30 = (bf16[2,16,1024]{2,1,0:T(8,128)(2,1)S(1)}, bf16[2,16,1024]{2,1,0:T(8,128)(2,1)S(1)}, u32[]{:S(2)}, u32[]{:S(2)}) collective-permute-start(bf16[2,16,1024]{2,1,0:T(8,128)(2,1)S(1)} %fusion.27), channel_id=1, source_target_pairs={{0,2},{2,0},{4,6},{6,4},{8,10},{10,8},{12,14},{14,12},{1,3},{3,1},... | collective-permute-start | bytes 196616 | tf_op jit(solution)/shard_map/ppermute | solution.py:18
  70.5 5.5 %collective-permute-start.33 = (bf16[2,16,1024]{2,1,0:T(8,128)(2,1)S(1)}, bf16[2,16,1024]{2,1,0:T(8,128)(2,1)S(1)}, u32[]{:S(2)}, u32[]{:S(2)}) collective-permute-start(bf16[2,16,1024]{2,1,0:T(8,128)(2,1)S(1)} %fusion.28), channel_id=1, source_target_pairs={{0,4},{2,6},{4,0},{6,2},{8,12},{10,14},{12,8},{14,10},{1,5},{3,7},... | collective-permute-start | bytes 196616 | tf_op jit(solution)/shard_map/ppermute | solution.py:18
  71.3 6.4 %collective-permute-start.36 = (bf16[2,16,1024]{2,1,0:T(8,128)(2,1)S(1)}, bf16[2,16,1024]{2,1,0:T(8,128)(2,1)S(1)}, u32[]{:S(2)}, u32[]{:S(2)}) collective-permute-start(bf16[2,16,1024]{2,1,0:T(8,128)(2,1)S(1)} %fusion.29), channel_id=1, source_target_pairs={{0,2},{2,0},{4,6},{6,4},{8,10},{10,8},{12,14},{14,12},{1,3},{3,1},... | collective-permute-start | bytes 196616 | tf_op jit(solution)/shard_map/ppermute | solution.py:18
  72.9 6.3 %collective-permute-start.28 = (bf16[16,1024]{1,0:T(8,128)(2,1)S(1)}, bf16[16,1024]{1,0:T(8,128)(2,1)S(1)}, u32[]{:S(2)}, u32[]{:S(2)}) collective-permute-start(bf16[16,1024]{1,0:T(8,128)(2,1)S(1)} %fusion.34), channel_id=1, source_target_pairs={{0,8},{2,10},{4,12},{6,14},{8,0},{10,2},{12,4},{14,6},{1,9},{3,11}... | collective-permute-start | bytes 98312 | tf_op jit(solution)/shard_map/ppermute | solution.py:18
  74.6 5.6 %collective-permute-start.31 = (bf16[16,1024]{1,0:T(8,128)(2,1)S(1)}, bf16[16,1024]{1,0:T(8,128)(2,1)S(1)}, u32[]{:S(2)}, u32[]{:S(2)}) collective-permute-start(bf16[16,1024]{1,0:T(8,128)(2,1)S(1)} %fusion.35), channel_id=1, source_target_pairs={{0,8},{2,10},{4,12},{6,14},{8,0},{10,2},{12,4},{14,6},{1,9},{3,11}... | collective-permute-start | bytes 98312 | tf_op jit(solution)/shard_map/ppermute | solution.py:18
  76.0 4.9 %collective-permute-start.34 = (bf16[16,1024]{1,0:T(8,128)(2,1)S(1)}, bf16[16,1024]{1,0:T(8,128)(2,1)S(1)}, u32[]{:S(2)}, u32[]{:S(2)}) collective-permute-start(bf16[16,1024]{1,0:T(8,128)(2,1)S(1)} %fusion.36), channel_id=1, source_target_pairs={{0,8},{2,10},{4,12},{6,14},{8,0},{10,2},{12,4},{14,6},{1,9},{3,11}... | collective-permute-start | bytes 98312 | tf_op jit(solution)/shard_map/ppermute | solution.py:18
  77.8 5.2 %collective-permute-start.37 = (bf16[16,1024]{1,0:T(8,128)(2,1)S(1)}, bf16[16,1024]{1,0:T(8,128)(2,1)S(1)}, u32[]{:S(2)}, u32[]{:S(2)}) collective-permute-start(bf16[16,1024]{1,0:T(8,128)(2,1)S(1)} %fusion.37), channel_id=1, source_target_pairs={{0,8},{2,10},{4,12},{6,14},{8,0},{10,2},{12,4},{14,6},{1,9},{3,11}... | collective-permute-start | bytes 98312 | tf_op jit(solution)/shard_map/ppermute | solution.py:18

commit v22 on v15

--- a/solution.py
+++ b/solution.py
@@ -42,19 +42,22 @@
     return value
 
 
-def scatter_sum(value, axis, order):
-    rows, cols = value.shape[0] >> len(order), value.shape[1]
-    total = value.reshape([2] * len(order) + [rows, cols])
-    left = sorted(order, reverse=True)
-    for bit in order:
-        dim = left.index(bit)
-        left.remove(bit)
-        low = lax.index_in_dim(total, 0, dim, keepdims=False)
-        high = lax.index_in_dim(total, 1, dim, keepdims=False)
+def scatter_sum(own, sends, axis):
+    groups = lax.axis_size(axis) // 4
+    total = own
+    for distance, send in enumerate(sends, 1):
+        total = total + swap(send, axis, distance).astype(jnp.float32)
+    bit = 2
+    while groups > 1:
+        groups //= 2
+        view = total.reshape(groups, 2, total.shape[0] // (2 * groups), total.shape[1])
+        low, high = view[:, 0], view[:, 1]
         upper = bit_of(axis, bit) == 1
-        send = jnp.where(upper, low, high).astype(jnp.bfloat16)
-        landed = swap(send, axis, 1 << bit)
-        total = jnp.where(upper, high, low) + landed.astype(jnp.float32)
+        landed = swap(jnp.where(upper, low, high).astype(jnp.bfloat16), axis, 1 << bit)
+        total = (jnp.where(upper, high, low) + landed.astype(jnp.float32)).reshape(
+            -1, total.shape[1]
+        )
+        bit += 1
     return total
 
 
@@ -159,9 +162,10 @@
     )
 
 
-def gram_kernel(total_cols, mine_ref, other_ref, packed_ref):
+def gram_kernel(total_cols, mine_ref, other_ref, packed_ref, sketch_ref):
     sketch = (mine_ref[...] + other_ref[...]) / total_cols
-    gram = matmul(sketch.T, sketch)
+    sketch_ref[...] = sketch.T
+    gram = matmul(sketch_ref[...], sketch)
     half = gram.shape[0] // 2
     row = lax.broadcasted_iota(jnp.int32, (half, 2 * half), 0)
     col = lax.broadcasted_iota(jnp.int32, (half, 2 * half), 1)
@@ -189,9 +193,12 @@
     rows, width = mine.shape
     return pl.pallas_call(
         functools.partial(gram_kernel, total_cols),
-        out_shape=jax.ShapeDtypeStruct((width // 2 + 8, width), jnp.float32),
+        out_shape=[
+            jax.ShapeDtypeStruct((width // 2 + 8, width), jnp.float32),
+            jax.ShapeDtypeStruct((width, rows), jnp.float32),
+        ],
         in_specs=[pl.BlockSpec(memory_space=pltpu.VMEM)] * 2,
-        out_specs=pl.BlockSpec(memory_space=pltpu.VMEM),
+        out_specs=[pl.BlockSpec(memory_space=pltpu.VMEM)] * 2,
         compiler_params=pltpu.CompilerParams(vmem_limit_bytes=16 * 2**20),
         name="make_gram",
     )(mine, other)
@@ -203,10 +210,10 @@
 
 
 def basis_kernel(
-    total_cols, root_rows, gram_ref, mine_ref, other_ref, slab_ref,
-    basis_ref, *refs,
+    parts, root_rows, gram_ref, sketch_ref, slab_ref,
+    basis_ref, own_ref, send1_ref, send2_ref, send3_ref,
+    work_ref, inverse_ref, buffer, arrived,
 ):
-    products, (work_ref, inverse_ref, buffer, arrived) = refs[:-4], refs[-4:]
     fetch = pltpu.make_async_copy(slab_ref, buffer, arrived)
     fetch.start()
     width = gram_ref.shape[1]
@@ -254,34 +261,48 @@
         pivots = jnp.sum(jnp.where(on_diag, work_ref[...], 0.0), axis=1, keepdims=True)
         inverse_ref[...] = inverse_ref[...] * lax.rsqrt(pivots)
 
-    sketch = (mine_ref[...] + other_ref[...]) / total_cols
-    basis = matmul_t(sketch, inverse_ref[...]) * root_rows
-    basis_ref[...] = basis
+    basis = matmul(inverse_ref[...], sketch_ref[...]) * root_rows
     high = basis.astype(jnp.bfloat16)
     low = (basis - high.astype(jnp.float32)).astype(jnp.bfloat16)
-    pair = jnp.concatenate([high, low], axis=1).T
+
+    share = width // parts
+    quarter = width // 4
+    me = lax.rem(lax.axis_index("row"), 4)
+    distance, inner = row // quarter, row % quarter
+    source = (inner // share * 4 + (distance ^ me)) * share + inner % share
+    order = jnp.where(col == source, 1.0, 0.0).astype(jnp.bfloat16)
+    pair = jnp.concatenate(
+        [
+            jnp.dot(order, high, preferred_element_type=jnp.float32).astype(jnp.bfloat16),
+            jnp.dot(order, low, preferred_element_type=jnp.float32).astype(jnp.bfloat16),
+        ],
+        axis=0,
+    )
     fetch.wait()
     for start in range(0, buffer.shape[1], TILE):
-        both = lax.dot_general(
-            pair,
-            buffer[:, start : start + TILE],
-            (((1,), (0,)), ((), ())),
-            preferred_element_type=jnp.float32,
-        )
-        out, inner = divmod(start, products[0].shape[1])
-        products[out][:, inner : inner + TILE] = both[:width] + both[width:]
-
-
-def make_basis(gram, mine, other, slab, total_cols, root_rows, chunks):
-    rows, width = mine.shape
-    cols = slab.shape[1]
+        span = slice(start, start + TILE)
+        both = jnp.dot(pair, buffer[:, span], preferred_element_type=jnp.float32)
+        product = both[:width] + both[width:]
+        own_ref[:, span] = product[:quarter]
+        for out_ref, begin in ((send1_ref, 1), (send2_ref, 2), (send3_ref, 3)):
+            block = product[begin * quarter : (begin + 1) * quarter]
+            out_ref[:, span] = block.astype(jnp.bfloat16)
+    basis_ref[...] = basis.T
+
+
+def make_basis(gram, sketch, slab, root_rows):
+    width, rows = sketch.shape
+    block = (width // 4, slab.shape[1])
     return pl.pallas_call(
-        functools.partial(basis_kernel, total_cols, root_rows),
-        out_shape=[jax.ShapeDtypeStruct((rows, width), jnp.float32)]
-        + [jax.ShapeDtypeStruct((width, cols // chunks), jnp.float32)] * chunks,
-        in_specs=[pl.BlockSpec(memory_space=pltpu.VMEM)] * 3
+        functools.partial(basis_kernel, lax.axis_size("row"), root_rows),
+        out_shape=[
+            jax.ShapeDtypeStruct((rows, width), jnp.float32),
+            jax.ShapeDtypeStruct(block, jnp.float32),
+        ]
+        + [jax.ShapeDtypeStruct(block, jnp.bfloat16)] * 3,
+        in_specs=[pl.BlockSpec(memory_space=pltpu.VMEM)] * 2
         + [pl.BlockSpec(memory_space=pl.ANY)],
-        out_specs=[pl.BlockSpec(memory_space=pltpu.VMEM)] * (1 + chunks),
+        out_specs=[pl.BlockSpec(memory_space=pltpu.VMEM)] * 5,
         scratch_shapes=[
             pltpu.VMEM((width, width), jnp.float32),
             pltpu.VMEM((width, width), jnp.float32),
@@ -290,7 +311,7 @@
         ],
         compiler_params=pltpu.CompilerParams(vmem_limit_bytes=KERNEL_VMEM),
         name="make_basis",
-    )(gram, mine, other, slab)
+    )(gram, sketch, slab)
 
 
 def per_device(activations, start_sketch):
@@ -315,16 +336,10 @@
             preferred_element_type=jnp.float32,
         )
     other_sketch = swap(partial_sketch, "col", 1)
-    gram = row_sum(make_gram(partial_sketch, other_sketch, total_cols))
-    basis, *products = make_basis(
-        gram, partial_sketch, other_sketch, activations, total_cols, root_rows, CHUNKS
-    )
-
-    pieces = [
-        scatter_sum(product, "row", orders[c % 2]) / total_rows
-        for c, product in enumerate(products)
-    ]
-    return (basis, jnp.concatenate(pieces, axis=1))
+    packed, sketch = make_gram(partial_sketch, other_sketch, total_cols)
+    basis, own, *sends = make_basis(row_sum(packed), sketch, activations, root_rows)
+    projection = scatter_sum(own, sends, "row") / total_rows
+    return (basis, projection)
 
 
 def solution(mesh):

time: 82.8 us -> 85.7 us (1.035)
  waiting for transfers between devices: 19.5 us -> 33.4 us
  starting transfers between devices: 49 us -> 38 us
    ppermute x34 -> x26, waiting for transfers between devices: 17 us -> 30 us  [swap(): return lax.ppermute(value, axis, [(i, i ^ distance) for i in range(size)])]
    ppermute x34 -> x26, starting transfers between devices: 43.9 us -> 32.9 us  [swap(): return lax.ppermute(value, axis, [(i, i ^ distance) for i in range(size)])]
    ppermute x4, waiting for transfers between devices: 2.47 us -> 3.45 us  [row_sum(): terms.append(lax.ppermute(value, ('row', 'col'), pairs))]
  transfers between devices with their start and end apart: 38 -> 30, of which waited for: 18 -> 19; matrix products, arithmetic and copies ran while one was open for 3% -> 2% of each run, Pallas kernels for 0% -> 0%
where the time goes in v22:
time: 85.7 us; the launch traced here: 85.5 us
  starting transfers between devices  38 us (44%)
  waiting for transfers between devices  33.4 us (39%)
  Pallas kernels  8.64 us (10%)
  other arithmetic  1.8 us (2%)
  matrix products  1.76 us (2%)
  between operations  0.94 us (1%)
  local copies, waits for them, and re-layouts  0.9 us (1%)
    ppermute x26, starting transfers between devices, swap(): return lax.ppermute(value, axis, [(i, i ^ distance) for i in range(size)])  32.9 us
    ppermute x26, waiting for transfers between devices, swap(): return lax.ppermute(value, axis, [(i, i ^ distance) for i in range(size)])  30 us
    pallas_call x1, Pallas kernels, make_basis(): pl.pallas_call(functools.partial(basis_kernel, lax.axis_size('row'), root...  5.14 us
    ppermute x4, starting transfers between devices, row_sum(): terms.append(lax.ppermute(value, ('row', 'col'), pairs))  5.1 us
    ppermute x4, waiting for transfers between devices, row_sum(): terms.append(lax.ppermute(value, ('row', 'col'), pairs))  3.45 us
    pallas_call x1, Pallas kernels, first_product(): pl.pallas_call(sketch_kernel, out_shape=[jax.ShapeDtypeStruct((width, col...  2.99 us
    dot_general x4, matrix products, per_device(): lax.dot_general(activations[:, span], shared, (((1,), (1,)), ((), ())), p...  1.76 us
  transfers between devices with their start and end apart: 30, of which 19 were waited for; matrix products, arithmetic and copies ran while one was open for 2% of the time, Pallas kernels for 0%

profile of v22, /device:TPU:0, one launch (start us, length us, event | category | flops | bytes accessed | tf_op | source)
XLA Modules:
  0.0 85.5 jit_solution(2742414246944443054)
XLA Ops:
  0.7 0.9 %copy-done = bf16[512,128]{1,0:T(8,128)(2,1)S(1)} copy-done((bf16[512,128]{1,0:T(8,128)(2,1)S(1)}, bf16[512,128]{1,0:T(8,128)(2,1)}, u32[]{:S(2)}) %copy-start) | copy-done | bytes 131096
  1.6 3.0 %first_product.1 = (f32[128,1024]{1,0:T(8,128)S(1)}, f32[128,1024]{1,0:T(8,128)S(1)}, f32[128,1024]{1,0:T(8,128)S(1)}, f32[128,1024]{1,0:T(8,128)S(1)}) custom-call(bf16[512,128]{1,0:T(8,128)(2,1)S(1)} %copy-done, bf16[512,4096]{1,0:T(8,128)(2,1)} %slab_ref.3), custom_call_target="tpu_custom_call" | custom-call | flops 536870912 | bytes 4194304 | tf_op jit(solution)/shard_map/first_product/pallas_call | solution.py:121
  4.6 3.1 %collective-permute-start.15 = (bf16[128,512]{1,0:T(8,128)(2,1)S(1)}, bf16[128,512]{1,0:T(8,128)(2,1)S(1)}, u32[]{:S(2)}, u32[]{:S(2)}) collective-permute-start(bf16[128,512]{1,0:T(8,128)(2,1)S(1)} %select_convert_fusion.1), channel_id=1, source_target_pairs={{0,4},{2,6},{4,0},{6,2},{8,12},{10,14},{12,8},{14,10},{1,5},{3,7},... | collective-permute-start | bytes 393224 | tf_op jit(solution)/shard_map/ppermute | solution.py:18
  7.7 1.6 %collective-permute-start.10 = (bf16[128,512]{1,0:T(8,128)(2,1)S(1)}, bf16[128,512]{1,0:T(8,128)(2,1)S(1)}, u32[]{:S(2)}, u32[]{:S(2)}) collective-permute-start(bf16[128,512]{1,0:T(8,128)(2,1)S(1)} %select_convert_fusion.2), channel_id=1, source_target_pairs={{0,2},{2,0},{4,6},{6,4},{8,10},{10,8},{12,14},{14,12},{1,3},{3,1},... | collective-permute-start | bytes 393224 | tf_op jit(solution)/shard_map/ppermute | solution.py:18
  9.3 0.5 collective-permute-start.5
  10.0 1.6 %collective-permute-done.15 = bf16[128,512]{1,0:T(8,128)(2,1)S(1)} collective-permute-done((bf16[128,512]{1,0:T(8,128)(2,1)S(1)}, bf16[128,512]{1,0:T(8,128)(2,1)S(1)}, u32[]{:S(2)}, u32[]{:S(2)}) %collective-permute-start.15) | collective-permute-done | bytes 131104 | tf_op jit(solution)/shard_map/ppermute | solution.py:18
  11.7 2.4 %collective-permute-start.16 = (bf16[128,256]{1,0:T(8,128)(2,1)S(1)}, bf16[128,256]{1,0:T(8,128)(2,1)S(1)}, u32[]{:S(2)}, u32[]{:S(2)}) collective-permute-start(bf16[128,256]{1,0:T(8,128)(2,1)S(1)} %select_convert_fusion.5), channel_id=1, source_target_pairs={{0,2},{2,0},{4,6},{6,4},{8,10},{10,8},{12,14},{14,12},{1,3},{3,1},... | collective-permute-start | bytes 196616 | tf_op jit(solution)/shard_map/ppermute | solution.py:18
  14.1 1.7 %collective-permute-start.11 = (bf16[128,256]{1,0:T(8,128)(2,1)S(1)}, bf16[128,256]{1,0:T(8,128)(2,1)S(1)}, u32[]{:S(2)}, u32[]{:S(2)}) collective-permute-start(bf16[128,256]{1,0:T(8,128)(2,1)S(1)} %select_convert_fusion.6), channel_id=1, source_target_pairs={{0,4},{2,6},{4,0},{6,2},{8,12},{10,14},{12,8},{14,10},{1,5},{3,7},... | collective-permute-start | bytes 196616 | tf_op jit(solution)/shard_map/ppermute | solution.py:18
  15.9 0.6 collective-permute-start.6
  16.7 1.5 %collective-permute-start.1 = (bf16[128,256]{1,0:T(8,128)(2,1)S(1)}, bf16[128,256]{1,0:T(8,128)(2,1)S(1)}, u32[]{:S(2)}, u32[]{:S(2)}) collective-permute-start(bf16[128,256]{1,0:T(8,128)(2,1)S(1)} %select_convert_fusion.8), channel_id=1, source_target_pairs={{0,4},{2,6},{4,0},{6,2},{8,12},{10,14},{12,8},{14,10},{1,5},{3,7},... | collective-permute-start | bytes 196616 | tf_op jit(solution)/shard_map/ppermute | solution.py:18
  18.2 2.7 %collective-permute-start.17 = (bf16[128,256]{1,0:T(8,128)(2,1)S(1)}, bf16[128,256]{1,0:T(8,128)(2,1)S(1)}, u32[]{:S(2)}, u32[]{:S(2)}) collective-permute-start(bf16[128,256]{1,0:T(8,128)(2,1)S(1)} %fusion.28), channel_id=1, source_target_pairs={{0,8},{2,10},{4,12},{6,14},{8,0},{10,2},{12,4},{14,6},{1,9},{3,11}... | collective-permute-start | bytes 196616 | tf_op jit(solution)/shard_map/ppermute | solution.py:18
  20.9 0.9 %collective-permute-start.12 = (bf16[128,256]{1,0:T(8,128)(2,1)S(1)}, bf16[128,256]{1,0:T(8,128)(2,1)S(1)}, u32[]{:S(2)}, u32[]{:S(2)}) collective-permute-start(bf16[128,256]{1,0:T(8,128)(2,1)S(1)} %fusion.27), channel_id=1, source_target_pairs={{0,8},{2,10},{4,12},{6,14},{8,0},{10,2},{12,4},{14,6},{1,9},{3,11}... | collective-permute-start | bytes 196616 | tf_op jit(solution)/shard_map/ppermute | solution.py:18
  21.8 2.2 %collective-permute-start.7 = (bf16[128,256]{1,0:T(8,128)(2,1)S(1)}, bf16[128,256]{1,0:T(8,128)(2,1)S(1)}, u32[]{:S(2)}, u32[]{:S(2)}) collective-permute-start(bf16[128,256]{1,0:T(8,128)(2,1)S(1)} %fusion.26), channel_id=1, source_target_pairs={{0,8},{2,10},{4,12},{6,14},{8,0},{10,2},{12,4},{14,6},{1,9},{3,11}... | collective-permute-start | bytes 196616 | tf_op jit(solution)/shard_map/ppermute | solution.py:18
  24.0 0.9 %collective-permute-start.2 = (bf16[128,256]{1,0:T(8,128)(2,1)S(1)}, bf16[128,256]{1,0:T(8,128)(2,1)S(1)}, u32[]{:S(2)}, u32[]{:S(2)}) collective-permute-start(bf16[128,256]{1,0:T(8,128)(2,1)S(1)} %fusion.25), channel_id=1, source_target_pairs={{0,8},{2,10},{4,12},{6,14},{8,0},{10,2},{12,4},{14,6},{1,9},{3,11}... | collective-permute-start | bytes 196616 | tf_op jit(solution)/shard_map/ppermute | solution.py:18
  24.9 2.2 %collective-permute-done.17 = bf16[128,256]{1,0:T(8,128)(2,1)S(1)} collective-permute-done((bf16[128,256]{1,0:T(8,128)(2,1)S(1)}, bf16[128,256]{1,0:T(8,128)(2,1)S(1)}, u32[]{:S(2)}, u32[]{:S(2)}) %collective-permute-start.17) | collective-permute-done | bytes 65568 | tf_op jit(solution)/shard_map/ppermute | solution.py:18
  27.1 1.8 %collective-permute-start.18 = (bf16[128,256]{1,0:T(8,128)(2,1)S(1)}, bf16[128,256]{1,0:T(8,128)(2,1)S(1)}, u32[]{:S(2)}, u32[]{:S(2)}) collective-permute-start(bf16[128,256]{1,0:T(8,128)(2,1)S(1)} %multiply_convert_fusion), channel_id=1, source_target_pairs={{0,2},{2,0},{4,6},{6,4},{8,10},{10,8},{12,14},{14,12},{1,3},{3,1},... | collective-permute-start | bytes 196616 | tf_op jit(solution)/shard_map/ppermute | solution.py:18
  28.9 1.1 %collective-permute-done.12 = bf16[128,256]{1,0:T(8,128)(2,1)S(1)} collective-permute-done((bf16[128,256]{1,0:T(8,128)(2,1)S(1)}, bf16[128,256]{1,0:T(8,128)(2,1)S(1)}, u32[]{:S(2)}, u32[]{:S(2)}) %collective-permute-start.12) | collective-permute-done | bytes 65568 | tf_op jit(solution)/shard_map/ppermute | solution.py:18
  30.1 1.0 %collective-permute-done.7 = bf16[128,256]{1,0:T(8,128)(2,1)S(1)} collective-permute-done((bf16[128,256]{1,0:T(8,128)(2,1)S(1)}, bf16[128,256]{1,0:T(8,128)(2,1)S(1)}, u32[]{:S(2)}, u32[]{:S(2)}) %collective-permute-start.7) | collective-permute-done | bytes 65568 | tf_op jit(solution)/shard_map/ppermute | solution.py:18
  31.1 1.2 %collective-permute-start.8 = (bf16[128,256]{1,0:T(8,128)(2,1)S(1)}, bf16[128,256]{1,0:T(8,128)(2,1)S(1)}, u32[]{:S(2)}, u32[]{:S(2)}) collective-permute-start(bf16[128,256]{1,0:T(8,128)(2,1)S(1)} %multiply_convert_fusion.2), channel_id=1, source_target_pairs={{0,2},{2,0},{4,6},{6,4},{8,10},{10,8},{12,14},{14,12},{1,3},{3,1},... | collective-permute-start | bytes 196616 | tf_op jit(solution)/shard_map/ppermute | solution.py:18
  32.3 1.1 %collective-permute-start.3 = (bf16[128,256]{1,0:T(8,128)(2,1)S(1)}, bf16[128,256]{1,0:T(8,128)(2,1)S(1)}, u32[]{:S(2)}, u32[]{:S(2)}) collective-permute-start(bf16[128,256]{1,0:T(8,128)(2,1)S(1)} %multiply_convert_fusion.3), channel_id=1, source_target_pairs={{0,4},{2,6},{4,0},{6,2},{8,12},{10,14},{12,8},{14,10},{1,5},{3,7},... | collective-permute-start | bytes 196616 | tf_op jit(solution)/shard_map/ppermute | solution.py:18
  33.5 1.0 %collective-permute-start.19 = (bf16[128,512]{1,0:T(8,128)(2,1)S(1)}, bf16[128,512]{1,0:T(8,128)(2,1)S(1)}, u32[]{:S(2)}, u32[]{:S(2)}) collective-permute-start(bf16[128,512]{1,0:T(8,128)(2,1)S(1)} %pad_maximum_fusion.3), channel_id=1, source_target_pairs={{0,4},{2,6},{4,0},{6,2},{8,12},{10,14},{12,8},{14,10},{1,5},{3,7},... | collective-permute-start | bytes 393224 | tf_op jit(solution)/shard_map/ppermute | solution.py:18
  34.5 0.5 collective-permute-done.13
  35.0 1.2 %collective-permute-start.14 = (bf16[128,512]{1,0:T(8,128)(2,1)S(1)}, bf16[128,512]{1,0:T(8,128)(2,1)S(1)}, u32[]{:S(2)}, u32[]{:S(2)}) collective-permute-start(bf16[128,512]{1,0:T(8,128)(2,1)S(1)} %pad_maximum_fusion.2), channel_id=1, source_target_pairs={{0,2},{2,0},{4,6},{6,4},{8,10},{10,8},{12,14},{14,12},{1,3},{3,1},... | collective-permute-start | bytes 393224 | tf_op jit(solution)/shard_map/ppermute | solution.py:18
  36.3 0.9 %collective-permute-start.9 = (bf16[128,512]{1,0:T(8,128)(2,1)S(1)}, bf16[128,512]{1,0:T(8,128)(2,1)S(1)}, u32[]{:S(2)}, u32[]{:S(2)}) collective-permute-start(bf16[128,512]{1,0:T(8,128)(2,1)S(1)} %pad_maximum_fusion.1), channel_id=1, source_target_pairs={{0,4},{2,6},{4,0},{6,2},{8,12},{10,14},{12,8},{14,10},{1,5},{3,7},... | collective-permute-start | bytes 393224 | tf_op jit(solution)/shard_map/ppermute | solution.py:18
  37.5 1.1 %collective-permute-start.4 = (bf16[128,512]{1,0:T(8,128)(2,1)S(1)}, bf16[128,512]{1,0:T(8,128)(2,1)S(1)}, u32[]{:S(2)}, u32[]{:S(2)}) collective-permute-start(bf16[128,512]{1,0:T(8,128)(2,1)S(1)} %pad_maximum_fusion), channel_id=1, source_target_pairs={{0,2},{2,0},{4,6},{6,4},{8,10},{10,8},{12,14},{14,12},{1,3},{3,1},... | collective-permute-start | bytes 393224 | tf_op jit(solution)/shard_map/ppermute | solution.py:18
  38.5 1.4 %collective-permute-done.19 = bf16[128,512]{1,0:T(8,128)(2,1)S(1)} collective-permute-done((bf16[128,512]{1,0:T(8,128)(2,1)S(1)}, bf16[128,512]{1,0:T(8,128)(2,1)S(1)}, u32[]{:S(2)}, u32[]{:S(2)}) %collective-permute-start.19) | collective-permute-done | bytes 131104 | tf_op jit(solution)/shard_map/ppermute | solution.py:18
  40.0 0.4 fusion.3
  41.4 0.4 fusion.7
  41.9 0.7 collective-permute-done.4
  42.6 0.4 fusion.2.mine_ref
  43.1 1.5 %collective-permute-done.20.other_ref = f32[512,128]{1,0:T(8,128)S(1)} collective-permute-done((f32[512,128]{1,0:T(8,128)S(1)}, f32[512,128]{1,0:T(8,128)S(1)}, u32[]{:S(2)}, u32[]{:S(2)}) %collective-permute-start.20) | collective-permute-done | bytes 262176 | tf_op jit(solution)/shard_map/ppermute | solution.py:18
  44.6 0.5 make_gram.1
  45.1 1.9 %collective-permute-start.23 = (f32[72,128]{1,0:T(8,128)S(1)}, f32[72,128]{1,0:T(8,128)S(1)}, u32[]{:S(2)}, u32[]{:S(2)}) collective-permute-start(f32[72,128]{1,0:T(8,128)S(1)} %get-tuple-element.17), channel_id=1, source_target_pairs={{0,8},{1,13},{2,10},{3,15},{4,12},{5,9},{6,14},{7,11},{8,0},{9,5},... | collective-permute-start | bytes 110600 | tf_op jit(solution)/shard_map/ppermute | solution.py:36
  47.0 1.5 %collective-permute-start.24 = (f32[72,128]{1,0:T(8,128)S(1)}, f32[72,128]{1,0:T(8,128)S(1)}, u32[]{:S(2)}, u32[]{:S(2)}) collective-permute-start(f32[72,128]{1,0:T(8,128)S(1)} %get-tuple-element.17), channel_id=1, source_target_pairs={{0,10},{1,15},{2,8},{3,13},{4,14},{5,11},{6,12},{7,9},{8,2},{9,7},... | collective-permute-start | bytes 110600 | tf_op jit(solution)/shard_map/ppermute | solution.py:36
  48.5 1.0 %collective-permute-start.22 = (f32[72,128]{1,0:T(8,128)S(1)}, f32[72,128]{1,0:T(8,128)S(1)}, u32[]{:S(2)}, u32[]{:S(2)}) collective-permute-start(f32[72,128]{1,0:T(8,128)S(1)} %get-tuple-element.17), channel_id=1, source_target_pairs={{0,2},{1,7},{2,0},{3,5},{4,6},{5,3},{6,4},{7,1},{8,10},{9,15},{10,... | collective-permute-start | bytes 110600 | tf_op jit(solution)/shard_map/ppermute | solution.py:36
  49.6 0.7 collective-permute-start.21
  50.2 0.9 %collective-permute-done.23 = f32[72,128]{1,0:T(8,128)S(1)} collective-permute-done((f32[72,128]{1,0:T(8,128)S(1)}, f32[72,128]{1,0:T(8,128)S(1)}, u32[]{:S(2)}, u32[]{:S(2)}) %collective-permute-start.23) | collective-permute-done | bytes 36896 | tf_op jit(solution)/shard_map/ppermute | solution.py:36
  51.1 2.3 %collective-permute-done.24 = f32[72,128]{1,0:T(8,128)S(1)} collective-permute-done((f32[72,128]{1,0:T(8,128)S(1)}, f32[72,128]{1,0:T(8,128)S(1)}, u32[]{:S(2)}, u32[]{:S(2)}) %collective-permute-start.24) | collective-permute-done | bytes 36896 | tf_op jit(solution)/shard_map/ppermute | solution.py:36
  53.7 0.6 collective-permute-start.25
  54.3 0.9 %collective-permute-done.25 = f32[72,128]{1,0:T(8,128)S(1)} collective-permute-done((f32[72,128]{1,0:T(8,128)S(1)}, f32[72,128]{1,0:T(8,128)S(1)}, u32[]{:S(2)}, u32[]{:S(2)}) %collective-permute-start.25) | collective-permute-done | bytes 36896 | tf_op jit(solution)/shard_map/ppermute | solution.py:18
  55.1 5.1 %make_basis.1 = (f32[512,128]{1,0:T(8,128)}, f32[32,4096]{1,0:T(8,128)S(1)}, bf16[32,4096]{1,0:T(8,128)(2,1)S(1)}, bf16[32,4096]{1,0:T(8,128)(2,1)S(1)}, bf16[32,4096]{1,0:T(8,128)(2,1)S(1)}) custom-call(f32[72,128]{1,0:T(8,128)S(1)} %add.92.gram_ref, f32[128,512]{1,0:T(8,128)S(1)} %get-tuple-element.18.sketch_ref, bf16[512,4096]{1,0:T(8,128)(2,1)} %slab_ref.3), custom_call_target="tpu_custom_call" | custom-call | tf_op jit(solution)/shard_map/make_basis/pallas_call | solution.py:296
  60.3 2.2 %collective-permute-start.28 = (bf16[32,4096]{1,0:T(8,128)(2,1)S(1)}, bf16[32,4096]{1,0:T(8,128)(2,1)S(1)}, u32[]{:S(2)}, u32[]{:S(2)}) collective-permute-start(bf16[32,4096]{1,0:T(8,128)(2,1)S(1)} %get-tuple-element.23), channel_id=1, source_target_pairs={{0,6},{2,4},{4,2},{6,0},{8,14},{10,12},{12,10},{14,8},{1,7},{3,5},... | collective-permute-start | bytes 786440 | tf_op jit(solution)/shard_map/ppermute | solution.py:18
  62.8 1.0 %collective-permute-start.26 = (bf16[32,4096]{1,0:T(8,128)(2,1)S(1)}, bf16[32,4096]{1,0:T(8,128)(2,1)S(1)}, u32[]{:S(2)}, u32[]{:S(2)}) collective-permute-start(bf16[32,4096]{1,0:T(8,128)(2,1)S(1)} %get-tuple-element.21), channel_id=1, source_target_pairs={{0,2},{2,0},{4,6},{6,4},{8,10},{10,8},{12,14},{14,12},{1,3},{3,1},... | collective-permute-start | bytes 786440 | tf_op jit(solution)/shard_map/ppermute | solution.py:18
  63.9 6.6 %collective-permute-done.28 = bf16[32,4096]{1,0:T(8,128)(2,1)S(1)} collective-permute-done((bf16[32,4096]{1,0:T(8,128)(2,1)S(1)}, bf16[32,4096]{1,0:T(8,128)(2,1)S(1)}, u32[]{:S(2)}, u32[]{:S(2)}) %collective-permute-start.28) | collective-permute-done | bytes 262176 | tf_op jit(solution)/shard_map/ppermute | solution.py:18
  70.4 4.6 %collective-permute-done.27 = bf16[32,4096]{1,0:T(8,128)(2,1)S(1)} collective-permute-done((bf16[32,4096]{1,0:T(8,128)(2,1)S(1)}, bf16[32,4096]{1,0:T(8,128)(2,1)S(1)}, u32[]{:S(2)}, u32[]{:S(2)}) %collective-permute-start.27) | collective-permute-done | bytes 262176 | tf_op jit(solution)/shard_map/ppermute | solution.py:18
  75.6 2.2 %collective-permute-start.29 = (bf16[1,16,4096]{2,1,0:T(8,128)(2,1)S(1)}, bf16[1,16,4096]{2,1,0:T(8,128)(2,1)S(1)}, u32[]{:S(2)}, u32[]{:S(2)}) collective-permute-start(bf16[1,16,4096]{2,1,0:T(8,128)(2,1)S(1)} %fusion.24), channel_id=1, source_target_pairs={{0,8},{2,10},{4,12},{6,14},{8,0},{10,2},{12,4},{14,6},{1,9},{3,11}... | collective-permute-start | bytes 393224 | tf_op jit(solution)/shard_map/ppermute | solution.py:18
  77.8 7.0 %collective-permute-done.29 = bf16[1,16,4096]{2,1,0:T(8,128)(2,1)S(1)} collective-permute-done((bf16[1,16,4096]{2,1,0:T(8,128)(2,1)S(1)}, bf16[1,16,4096]{2,1,0:T(8,128)(2,1)S(1)}, u32[]{:S(2)}, u32[]{:S(2)}) %collective-permute-start.29) | collective-permute-done | bytes 131104 | tf_op jit(solution)/shard_map/ppermute | solution.py:18
  84.8 0.8 fusion.23
  (60 shorter events, 3.4 us)
Async XLA Ops:
  0.6 0.9 %copy-start = (bf16[512,128]{1,0:T(8,128)(2,1)S(1)}, bf16[512,128]{1,0:T(8,128)(2,1)}, u32[]{:S(2)}) copy-start(bf16[512,128]{1,0:T(8,128)(2,1)} %start_ref.1) | copy-start | bytes 393220
  4.6 7.0 %collective-permute-start.15 = (bf16[128,512]{1,0:T(8,128)(2,1)S(1)}, bf16[128,512]{1,0:T(8,128)(2,1)S(1)}, u32[]{:S(2)}, u32[]{:S(2)}) collective-permute-start(bf16[128,512]{1,0:T(8,128)(2,1)S(1)} %select_convert_fusion.1), channel_id=1, source_target_pairs={{0,4},{2,6},{4,0},{6,2},{8,12},{10,14},{12,8},{14,10},{1,5},{3,7},... | collective-permute-start | bytes 393224 | tf_op jit(solution)/shard_map/ppermute | solution.py:18
  7.7 6.3 %collective-permute-start.10 = (bf16[128,512]{1,0:T(8,128)(2,1)S(1)}, bf16[128,512]{1,0:T(8,128)(2,1)S(1)}, u32[]{:S(2)}, u32[]{:S(2)}) collective-permute-start(bf16[128,512]{1,0:T(8,128)(2,1)S(1)} %select_convert_fusion.2), channel_id=1, source_target_pairs={{0,2},{2,0},{4,6},{6,4},{8,10},{10,8},{12,14},{14,12},{1,3},{3,1},... | collective-permute-start | bytes 393224 | tf_op jit(solution)/shard_map/ppermute | solution.py:18
  9.3 6.6 %collective-permute-start.5 = (bf16[128,512]{1,0:T(8,128)(2,1)S(1)}, bf16[128,512]{1,0:T(8,128)(2,1)S(1)}, u32[]{:S(2)}, u32[]{:S(2)}) collective-permute-start(bf16[128,512]{1,0:T(8,128)(2,1)S(1)} %select_convert_fusion.3), channel_id=1, source_target_pairs={{0,4},{2,6},{4,0},{6,2},{8,12},{10,14},{12,8},{14,10},{1,5},{3,7},... | collective-permute-start | bytes 393224 | tf_op jit(solution)/shard_map/ppermute | solution.py:18
  9.8 6.7 %collective-permute-start = (bf16[128,512]{1,0:T(8,128)(2,1)S(1)}, bf16[128,512]{1,0:T(8,128)(2,1)S(1)}, u32[]{:S(2)}, u32[]{:S(2)}) collective-permute-start(bf16[128,512]{1,0:T(8,128)(2,1)S(1)} %select_convert_fusion.4), channel_id=1, source_target_pairs={{0,2},{2,0},{4,6},{6,4},{8,10},{10,8},{12,14},{14,12},{1,3},{3,1},... | collective-permute-start | bytes 393224 | tf_op jit(solution)/shard_map/ppermute | solution.py:18
  11.7 6.5 %collective-permute-start.16 = (bf16[128,256]{1,0:T(8,128)(2,1)S(1)}, bf16[128,256]{1,0:T(8,128)(2,1)S(1)}, u32[]{:S(2)}, u32[]{:S(2)}) collective-permute-start(bf16[128,256]{1,0:T(8,128)(2,1)S(1)} %select_convert_fusion.5), channel_id=1, source_target_pairs={{0,2},{2,0},{4,6},{6,4},{8,10},{10,8},{12,14},{14,12},{1,3},{3,1},... | collective-permute-start | bytes 196616 | tf_op jit(solution)/shard_map/ppermute | solution.py:18
  14.1 25.9 %copy-start.1 = (bf16[512,4096]{1,0:T(8,128)(2,1)S(1)}, bf16[512,4096]{1,0:T(8,128)(2,1)}, u32[]{:S(2)}) copy-start(bf16[512,4096]{1,0:T(8,128)(2,1)} %slab_ref.3) | copy-start | bytes 12582916
  14.1 6.7 %collective-permute-start.11 = (bf16[128,256]{1,0:T(8,128)(2,1)S(1)}, bf16[128,256]{1,0:T(8,128)(2,1)S(1)}, u32[]{:S(2)}, u32[]{:S(2)}) collective-permute-start(bf16[128,256]{1,0:T(8,128)(2,1)S(1)} %select_convert_fusion.6), channel_id=1, source_target_pairs={{0,4},{2,6},{4,0},{6,2},{8,12},{10,14},{12,8},{14,10},{1,5},{3,7},... | collective-permute-start | bytes 196616 | tf_op jit(solution)/shard_map/ppermute | solution.py:18
  15.9 5.8 %collective-permute-start.6 = (bf16[128,256]{1,0:T(8,128)(2,1)S(1)}, bf16[128,256]{1,0:T(8,128)(2,1)S(1)}, u32[]{:S(2)}, u32[]{:S(2)}) collective-permute-start(bf16[128,256]{1,0:T(8,128)(2,1)S(1)} %select_convert_fusion.7), channel_id=1, source_target_pairs={{0,2},{2,0},{4,6},{6,4},{8,10},{10,8},{12,14},{14,12},{1,3},{3,1},... | collective-permute-start | bytes 196616 | tf_op jit(solution)/shard_map/ppermute | solution.py:18
  16.7 7.3 %collective-permute-start.1 = (bf16[128,256]{1,0:T(8,128)(2,1)S(1)}, bf16[128,256]{1,0:T(8,128)(2,1)S(1)}, u32[]{:S(2)}, u32[]{:S(2)}) collective-permute-start(bf16[128,256]{1,0:T(8,128)(2,1)S(1)} %select_convert_fusion.8), channel_id=1, source_target_pairs={{0,4},{2,6},{4,0},{6,2},{8,12},{10,14},{12,8},{14,10},{1,5},{3,7},... | collective-permute-start | bytes 196616 | tf_op jit(solution)/shard_map/ppermute | solution.py:18
  18.2 8.8 %collective-permute-start.17 = (bf16[128,256]{1,0:T(8,128)(2,1)S(1)}, bf16[128,256]{1,0:T(8,128)(2,1)S(1)}, u32[]{:S(2)}, u32[]{:S(2)}) collective-permute-start(bf16[128,256]{1,0:T(8,128)(2,1)S(1)} %fusion.28), channel_id=1, source_target_pairs={{0,8},{2,10},{4,12},{6,14},{8,0},{10,2},{12,4},{14,6},{1,9},{3,11}... | collective-permute-start | bytes 196616 | tf_op jit(solution)/shard_map/ppermute | solution.py:18
  20.9 9.1 %collective-permute-start.12 = (bf16[128,256]{1,0:T(8,128)(2,1)S(1)}, bf16[128,256]{1,0:T(8,128)(2,1)S(1)}, u32[]{:S(2)}, u32[]{:S(2)}) collective-permute-start(bf16[128,256]{1,0:T(8,128)(2,1)S(1)} %fusion.27), channel_id=1, source_target_pairs={{0,8},{2,10},{4,12},{6,14},{8,0},{10,2},{12,4},{14,6},{1,9},{3,11}... | collective-permute-start | bytes 196616 | tf_op jit(solution)/shard_map/ppermute | solution.py:18
  21.8 9.3 %collective-permute-start.7 = (bf16[128,256]{1,0:T(8,128)(2,1)S(1)}, bf16[128,256]{1,0:T(8,128)(2,1)S(1)}, u32[]{:S(2)}, u32[]{:S(2)}) collective-permute-start(bf16[128,256]{1,0:T(8,128)(2,1)S(1)} %fusion.26), channel_id=1, source_target_pairs={{0,8},{2,10},{4,12},{6,14},{8,0},{10,2},{12,4},{14,6},{1,9},{3,11}... | collective-permute-start | bytes 196616 | tf_op jit(solution)/shard_map/ppermute | solution.py:18
  24.0 8.3 %collective-permute-start.2 = (bf16[128,256]{1,0:T(8,128)(2,1)S(1)}, bf16[128,256]{1,0:T(8,128)(2,1)S(1)}, u32[]{:S(2)}, u32[]{:S(2)}) collective-permute-start(bf16[128,256]{1,0:T(8,128)(2,1)S(1)} %fusion.25), channel_id=1, source_target_pairs={{0,8},{2,10},{4,12},{6,14},{8,0},{10,2},{12,4},{14,6},{1,9},{3,11}... | collective-permute-start | bytes 196616 | tf_op jit(solution)/shard_map/ppermute | solution.py:18
  27.1 6.4 %collective-permute-start.18 = (bf16[128,256]{1,0:T(8,128)(2,1)S(1)}, bf16[128,256]{1,0:T(8,128)(2,1)S(1)}, u32[]{:S(2)}, u32[]{:S(2)}) collective-permute-start(bf16[128,256]{1,0:T(8,128)(2,1)S(1)} %multiply_convert_fusion), channel_id=1, source_target_pairs={{0,2},{2,0},{4,6},{6,4},{8,10},{10,8},{12,14},{14,12},{1,3},{3,1},... | collective-permute-start | bytes 196616 | tf_op jit(solution)/shard_map/ppermute | solution.py:18
  30.0 5.0 %collective-permute-start.13 = (bf16[128,256]{1,0:T(8,128)(2,1)S(1)}, bf16[128,256]{1,0:T(8,128)(2,1)S(1)}, u32[]{:S(2)}, u32[]{:S(2)}) collective-permute-start(bf16[128,256]{1,0:T(8,128)(2,1)S(1)} %multiply_convert_fusion.1), channel_id=1, source_target_pairs={{0,4},{2,6},{4,0},{6,2},{8,12},{10,14},{12,8},{14,10},{1,5},{3,7},... | collective-permute-start | bytes 196616 | tf_op jit(solution)/shard_map/ppermute | solution.py:18
  31.1 5.1 %collective-permute-start.8 = (bf16[128,256]{1,0:T(8,128)(2,1)S(1)}, bf16[128,256]{1,0:T(8,128)(2,1)S(1)}, u32[]{:S(2)}, u32[]{:S(2)}) collective-permute-start(bf16[128,256]{1,0:T(8,128)(2,1)S(1)} %multiply_convert_fusion.2), channel_id=1, source_target_pairs={{0,2},{2,0},{4,6},{6,4},{8,10},{10,8},{12,14},{14,12},{1,3},{3,1},... | collective-permute-start | bytes 196616 | tf_op jit(solution)/shard_map/ppermute | solution.py:18
  32.3 5.1 %collective-permute-start.3 = (bf16[128,256]{1,0:T(8,128)(2,1)S(1)}, bf16[128,256]{1,0:T(8,128)(2,1)S(1)}, u32[]{:S(2)}, u32[]{:S(2)}) collective-permute-start(bf16[128,256]{1,0:T(8,128)(2,1)S(1)} %multiply_convert_fusion.3), channel_id=1, source_target_pairs={{0,4},{2,6},{4,0},{6,2},{8,12},{10,14},{12,8},{14,10},{1,5},{3,7},... | collective-permute-start | bytes 196616 | tf_op jit(solution)/shard_map/ppermute | solution.py:18
  33.5 6.4 %collective-permute-start.19 = (bf16[128,512]{1,0:T(8,128)(2,1)S(1)}, bf16[128,512]{1,0:T(8,128)(2,1)S(1)}, u32[]{:S(2)}, u32[]{:S(2)}) collective-permute-start(bf16[128,512]{1,0:T(8,128)(2,1)S(1)} %pad_maximum_fusion.3), channel_id=1, source_target_pairs={{0,4},{2,6},{4,0},{6,2},{8,12},{10,14},{12,8},{14,10},{1,5},{3,7},... | collective-permute-start | bytes 393224 | tf_op jit(solution)/shard_map/ppermute | solution.py:18
  35.0 5.6 %collective-permute-start.14 = (bf16[128,512]{1,0:T(8,128)(2,1)S(1)}, bf16[128,512]{1,0:T(8,128)(2,1)S(1)}, u32[]{:S(2)}, u32[]{:S(2)}) collective-permute-start(bf16[128,512]{1,0:T(8,128)(2,1)S(1)} %pad_maximum_fusion.2), channel_id=1, source_target_pairs={{0,2},{2,0},{4,6},{6,4},{8,10},{10,8},{12,14},{14,12},{1,3},{3,1},... | collective-permute-start | bytes 393224 | tf_op jit(solution)/shard_map/ppermute | solution.py:18
  36.3 5.0 %collective-permute-start.9 = (bf16[128,512]{1,0:T(8,128)(2,1)S(1)}, bf16[128,512]{1,0:T(8,128)(2,1)S(1)}, u32[]{:S(2)}, u32[]{:S(2)}) collective-permute-start(bf16[128,512]{1,0:T(8,128)(2,1)S(1)} %pad_maximum_fusion.1), channel_id=1, source_target_pairs={{0,4},{2,6},{4,0},{6,2},{8,12},{10,14},{12,8},{14,10},{1,5},{3,7},... | collective-permute-start | bytes 393224 | tf_op jit(solution)/shard_map/ppermute | solution.py:18
  37.5 5.0 %collective-permute-start.4 = (bf16[128,512]{1,0:T(8,128)(2,1)S(1)}, bf16[128,512]{1,0:T(8,128)(2,1)S(1)}, u32[]{:S(2)}, u32[]{:S(2)}) collective-permute-start(bf16[128,512]{1,0:T(8,128)(2,1)S(1)} %pad_maximum_fusion), channel_id=1, source_target_pairs={{0,2},{2,0},{4,6},{6,4},{8,10},{10,8},{12,14},{14,12},{1,3},{3,1},... | collective-permute-start | bytes 393224 | tf_op jit(solution)/shard_map/ppermute | solution.py:18
  43.0 1.6 %collective-permute-start.20 = (f32[512,128]{1,0:T(8,128)S(1)}, f32[512,128]{1,0:T(8,128)S(1)}, u32[]{:S(2)}, u32[]{:S(2)}) collective-permute-start(f32[512,128]{1,0:T(8,128)S(1)} %fusion.2.mine_ref), channel_id=1, source_target_pairs={{0,1},{1,0},{2,3},{3,2},{4,5},{5,4},{6,7},{7,6},{8,9},{9,8},{10,11... | collective-permute-start | bytes 786440 | tf_op jit(solution)/shard_map/ppermute | solution.py:18
  45.1 6.0 %collective-permute-start.23 = (f32[72,128]{1,0:T(8,128)S(1)}, f32[72,128]{1,0:T(8,128)S(1)}, u32[]{:S(2)}, u32[]{:S(2)}) collective-permute-start(f32[72,128]{1,0:T(8,128)S(1)} %get-tuple-element.17), channel_id=1, source_target_pairs={{0,8},{1,13},{2,10},{3,15},{4,12},{5,9},{6,14},{7,11},{8,0},{9,5},... | collective-permute-start | bytes 110600 | tf_op jit(solution)/shard_map/ppermute | solution.py:36
  47.0 6.5 %collective-permute-start.24 = (f32[72,128]{1,0:T(8,128)S(1)}, f32[72,128]{1,0:T(8,128)S(1)}, u32[]{:S(2)}, u32[]{:S(2)}) collective-permute-start(f32[72,128]{1,0:T(8,128)S(1)} %get-tuple-element.17), channel_id=1, source_target_pairs={{0,10},{1,15},{2,8},{3,13},{4,14},{5,11},{6,12},{7,9},{8,2},{9,7},... | collective-permute-start | bytes 110600 | tf_op jit(solution)/shard_map/ppermute | solution.py:36
  48.5 5.1 %collective-permute-start.22 = (f32[72,128]{1,0:T(8,128)S(1)}, f32[72,128]{1,0:T(8,128)S(1)}, u32[]{:S(2)}, u32[]{:S(2)}) collective-permute-start(f32[72,128]{1,0:T(8,128)S(1)} %get-tuple-element.17), channel_id=1, source_target_pairs={{0,2},{1,7},{2,0},{3,5},{4,6},{5,3},{6,4},{7,1},{8,10},{9,15},{10,... | collective-permute-start | bytes 110600 | tf_op jit(solution)/shard_map/ppermute | solution.py:36
  49.6 4.1 %collective-permute-start.21 = (f32[72,128]{1,0:T(8,128)S(1)}, f32[72,128]{1,0:T(8,128)S(1)}, u32[]{:S(2)}, u32[]{:S(2)}) collective-permute-start(f32[72,128]{1,0:T(8,128)S(1)} %get-tuple-element.17), channel_id=1, source_target_pairs={{1,5},{3,7},{5,1},{7,3},{9,13},{11,15},{13,9},{15,11},{17,21},{19,... | collective-permute-start | bytes 110600 | tf_op jit(solution)/shard_map/ppermute | solution.py:36
  53.7 1.4 %collective-permute-start.25 = (f32[72,128]{1,0:T(8,128)S(1)}, f32[72,128]{1,0:T(8,128)S(1)}, u32[]{:S(2)}, u32[]{:S(2)}) collective-permute-start(f32[72,128]{1,0:T(8,128)S(1)} %add_add_fusion), channel_id=1, source_target_pairs={{0,1},{1,0},{2,3},{3,2},{4,5},{5,4},{6,7},{7,6},{8,9},{9,8},{10,11... | collective-permute-start | bytes 110600 | tf_op jit(solution)/shard_map/ppermute | solution.py:18
  60.3 10.1 %collective-permute-start.28 = (bf16[32,4096]{1,0:T(8,128)(2,1)S(1)}, bf16[32,4096]{1,0:T(8,128)(2,1)S(1)}, u32[]{:S(2)}, u32[]{:S(2)}) collective-permute-start(bf16[32,4096]{1,0:T(8,128)(2,1)S(1)} %get-tuple-element.23), channel_id=1, source_target_pairs={{0,6},{2,4},{4,2},{6,0},{8,14},{10,12},{12,10},{14,8},{1,7},{3,5},... | collective-permute-start | bytes 786440 | tf_op jit(solution)/shard_map/ppermute | solution.py:18
  62.5 12.5 %collective-permute-start.27 = (bf16[32,4096]{1,0:T(8,128)(2,1)S(1)}, bf16[32,4096]{1,0:T(8,128)(2,1)S(1)}, u32[]{:S(2)}, u32[]{:S(2)}) collective-permute-start(bf16[32,4096]{1,0:T(8,128)(2,1)S(1)} %get-tuple-element.22), channel_id=1, source_target_pairs={{0,4},{2,6},{4,0},{6,2},{8,12},{10,14},{12,8},{14,10},{1,5},{3,7},... | collective-permute-start | bytes 786440 | tf_op jit(solution)/shard_map/ppermute | solution.py:18
  62.8 12.6 %collective-permute-start.26 = (bf16[32,4096]{1,0:T(8,128)(2,1)S(1)}, bf16[32,4096]{1,0:T(8,128)(2,1)S(1)}, u32[]{:S(2)}, u32[]{:S(2)}) collective-permute-start(bf16[32,4096]{1,0:T(8,128)(2,1)S(1)} %get-tuple-element.21), channel_id=1, source_target_pairs={{0,2},{2,0},{4,6},{6,4},{8,10},{10,8},{12,14},{14,12},{1,3},{3,1},... | collective-permute-start | bytes 786440 | tf_op jit(solution)/shard_map/ppermute | solution.py:18
  75.6 9.2 %collective-permute-start.29 = (bf16[1,16,4096]{2,1,0:T(8,128)(2,1)S(1)}, bf16[1,16,4096]{2,1,0:T(8,128)(2,1)S(1)}, u32[]{:S(2)}, u32[]{:S(2)}) collective-permute-start(bf16[1,16,4096]{2,1,0:T(8,128)(2,1)S(1)} %fusion.24), channel_id=1, source_target_pairs={{0,8},{2,10},{4,12},{6,14},{8,0},{10,2},{12,4},{14,6},{1,9},{3,11}... | collective-permute-start | bytes 393224 | tf_op jit(solution)/shard_map/ppermute | solution.py:18

commit v23 on v15

--- a/solution.py
+++ b/solution.py
@@ -88,10 +88,10 @@
     return [bits, [bits[1], bits[0]] + bits[2:]]
 
 
-def fetch_tiles(slab_ref, buffer, arrived):
+def fetch_tiles(slab_ref, begin, buffer, arrived):
     copies = []
     for tile in range(buffer.shape[0]):
-        span = pl.ds(tile * TILE, TILE)
+        span = pl.ds(begin + tile * TILE, TILE)
         copies.append(
             pltpu.make_async_copy(slab_ref.at[:, span], buffer.at[tile], arrived.at[tile])
         )
@@ -100,9 +100,9 @@
     return copies
 
 
-def sketch_kernel(start_ref, slab_ref, *refs):
+def sketch_kernel(begin, start_ref, slab_ref, *refs):
     outs, (buffer, arrived) = refs[:-2], refs[-2:]
-    copies = fetch_tiles(slab_ref, buffer, arrived)
+    copies = fetch_tiles(slab_ref, begin, buffer, arrived)
     left = start_ref[...].T
     for tile, copy in enumerate(copies):
         copy.wait()
@@ -112,11 +112,10 @@
         )
 
 
-def first_product(start, slab, chunks):
+def first_product(start, slab, begin, cols, chunks):
     rows, width = start.shape
-    cols = slab.shape[1]
     return pl.pallas_call(
-        sketch_kernel,
+        functools.partial(sketch_kernel, begin),
         out_shape=[jax.ShapeDtypeStruct((width, cols // chunks), jnp.float32)] * chunks,
         in_specs=[
             pl.BlockSpec(memory_space=pltpu.VMEM),
@@ -301,7 +300,11 @@
     total_cols = cols_here * lax.axis_size("col")
     root_rows = math.sqrt(total_rows)
 
-    local_cols = first_product(start_sketch, activations, CHUNKS)
+    local_cols = []
+    for begin in (0, cols_here // 2):
+        local_cols += first_product(
+            start_sketch, activations, begin, cols_here // 2, CHUNKS // 2
+        )
     partial_sketch = 0.0
     orders = orders_of("row")
     step = cols_here // CHUNKS

time: 82.8 us -> 81.9 us (0.989)
  starting transfers between devices: 49 us -> 44.5 us
  waiting for transfers between devices: 19.5 us -> 22 us
  Pallas kernels: 8.11 us -> 9.19 us
    ppermute x34, starting transfers between devices: 43.9 us -> 39.4 us  [swap(): return lax.ppermute(value, axis, [(i, i ^ distance) for i in range(size)])]
    ppermute x34, waiting for transfers between devices: 17 us -> 19.3 us  [swap(): return lax.ppermute(value, axis, [(i, i ^ distance) for i in range(size)])]
    pallas_call x1 -> x2, Pallas kernels: 2.99 us -> 4.07 us  [first_product(): pl.pallas_call(functools.partial(sketch_kernel, begin), out_shape=[jax.Sh...]
  transfers between devices with their start and end apart: 38 -> 38, of which waited for: 18 -> 19; matrix products, arithmetic and copies ran while one was open for 3% -> 3% of each run, Pallas kernels for 0% -> 2%
where the time goes in v23:
time: 81.9 us; the launch traced here: 81.7 us
  starting transfers between devices  44.5 us (54%)
  waiting for transfers between devices  22 us (27%)
  Pallas kernels  9.19 us (11%)
  other arithmetic  2.15 us (3%)
  matrix products  1.74 us (2%)
  between operations  1.12 us (1%)
  local copies, waits for them, and re-layouts  1.05 us (1%)
    ppermute x34, starting transfers between devices, swap(): return lax.ppermute(value, axis, [(i, i ^ distance) for i in range(size)])  39.4 us
    ppermute x34, waiting for transfers between devices, swap(): return lax.ppermute(value, axis, [(i, i ^ distance) for i in range(size)])  19.3 us
    ppermute x4, starting transfers between devices, row_sum(): terms.append(lax.ppermute(value, ('row', 'col'), pairs))  5.1 us
    pallas_call x1, Pallas kernels, make_basis(): pl.pallas_call(functools.partial(basis_kernel, total_cols, root_rows), ou...  4.63 us
    pallas_call x2, Pallas kernels, first_product(): pl.pallas_call(functools.partial(sketch_kernel, begin), out_shape=[jax.Sh...  4.07 us
    ppermute x4, waiting for transfers between devices, row_sum(): terms.append(lax.ppermute(value, ('row', 'col'), pairs))  2.65 us
    dot_general x4, matrix products, per_device(): lax.dot_general(activations[:, span], shared, (((1,), (1,)), ((), ())), p...  1.74 us
  transfers between devices with their start and end apart: 38, of which 19 were waited for; matrix products, arithmetic and copies ran while one was open for 3% of the time, Pallas kernels for 2%

profile of v23, /device:TPU:0, one launch (start us, length us, event | category | flops | bytes accessed | tf_op | source)
XLA Modules:
  0.0 81.7 jit_solution(5393763483126511231)
XLA Ops:
  0.7 0.9 %copy-done = bf16[512,128]{1,0:T(8,128)(2,1)S(1)} copy-done((bf16[512,128]{1,0:T(8,128)(2,1)S(1)}, bf16[512,128]{1,0:T(8,128)(2,1)}, u32[]{:S(2)}) %copy-start) | copy-done | bytes 131096
  1.6 2.1 %first_product.3 = (f32[128,1024]{1,0:T(8,128)S(1)}, f32[128,1024]{1,0:T(8,128)S(1)}) custom-call(bf16[512,128]{1,0:T(8,128)(2,1)S(1)} %copy-done, bf16[512,4096]{1,0:T(8,128)(2,1)} %slab_ref.5), custom_call_target="tpu_custom_call" | custom-call | flops 268435456 | bytes 2097152 | tf_op jit(solution)/shard_map/first_product/pallas_call | solution.py:117
  3.6 3.1 %collective-permute-start.15 = (bf16[128,512]{1,0:T(8,128)(2,1)S(1)}, bf16[128,512]{1,0:T(8,128)(2,1)S(1)}, u32[]{:S(2)}, u32[]{:S(2)}) collective-permute-start(bf16[128,512]{1,0:T(8,128)(2,1)S(1)} %select_convert_fusion.4), channel_id=1, source_target_pairs={{0,4},{2,6},{4,0},{6,2},{8,12},{10,14},{12,8},{14,10},{1,5},{3,7},... | collective-permute-start | bytes 393224 | tf_op jit(solution)/shard_map/ppermute | solution.py:18
  6.8 1.6 %collective-permute-start.10 = (bf16[128,512]{1,0:T(8,128)(2,1)S(1)}, bf16[128,512]{1,0:T(8,128)(2,1)S(1)}, u32[]{:S(2)}, u32[]{:S(2)}) collective-permute-start(bf16[128,512]{1,0:T(8,128)(2,1)S(1)} %select_convert_fusion.5), channel_id=1, source_target_pairs={{0,2},{2,0},{4,6},{6,4},{8,10},{10,8},{12,14},{14,12},{1,3},{3,1},... | collective-permute-start | bytes 393224 | tf_op jit(solution)/shard_map/ppermute | solution.py:18
  8.3 2.0 %first_product.2 = (f32[128,1024]{1,0:T(8,128)S(1)}, f32[128,1024]{1,0:T(8,128)S(1)}) custom-call(bf16[512,128]{1,0:T(8,128)(2,1)S(1)} %copy-done.1, bf16[512,4096]{1,0:T(8,128)(2,1)} %slab_ref.5), custom_call_target="tpu_custom_call" | custom-call | flops 268435456 | bytes 2097152 | tf_op jit(solution)/shard_map/first_product/pallas_call | solution.py:117
  11.2 2.0 %collective-permute-start.16 = (bf16[128,256]{1,0:T(8,128)(2,1)S(1)}, bf16[128,256]{1,0:T(8,128)(2,1)S(1)}, u32[]{:S(2)}, u32[]{:S(2)}) collective-permute-start(bf16[128,256]{1,0:T(8,128)(2,1)S(1)} %select_convert_fusion.12), channel_id=1, source_target_pairs={{0,2},{2,0},{4,6},{6,4},{8,10},{10,8},{12,14},{14,12},{1,3},{3,1},... | collective-permute-start | bytes 196616 | tf_op jit(solution)/shard_map/ppermute | solution.py:18
  13.3 1.6 %collective-permute-start.11 = (bf16[128,256]{1,0:T(8,128)(2,1)S(1)}, bf16[128,256]{1,0:T(8,128)(2,1)S(1)}, u32[]{:S(2)}, u32[]{:S(2)}) collective-permute-start(bf16[128,256]{1,0:T(8,128)(2,1)S(1)} %select_convert_fusion.13), channel_id=1, source_target_pairs={{0,4},{2,6},{4,0},{6,2},{8,12},{10,14},{12,8},{14,10},{1,5},{3,7},... | collective-permute-start | bytes 196616 | tf_op jit(solution)/shard_map/ppermute | solution.py:18
  14.9 1.2 %collective-permute-done.5 = bf16[128,512]{1,0:T(8,128)(2,1)S(1)} collective-permute-done((bf16[128,512]{1,0:T(8,128)(2,1)S(1)}, bf16[128,512]{1,0:T(8,128)(2,1)S(1)}, u32[]{:S(2)}, u32[]{:S(2)}) %collective-permute-start.5) | collective-permute-done | bytes 131104 | tf_op jit(solution)/shard_map/ppermute | solution.py:18
  16.2 0.6 collective-permute-start.6
  16.9 1.6 %collective-permute-start.1 = (bf16[128,256]{1,0:T(8,128)(2,1)S(1)}, bf16[128,256]{1,0:T(8,128)(2,1)S(1)}, u32[]{:S(2)}, u32[]{:S(2)}) collective-permute-start(bf16[128,256]{1,0:T(8,128)(2,1)S(1)} %select_convert_fusion.15), channel_id=1, source_target_pairs={{0,4},{2,6},{4,0},{6,2},{8,12},{10,14},{12,8},{14,10},{1,5},{3,7},... | collective-permute-start | bytes 196616 | tf_op jit(solution)/shard_map/ppermute | solution.py:18
  18.5 2.7 %collective-permute-start.17 = (bf16[128,256]{1,0:T(8,128)(2,1)S(1)}, bf16[128,256]{1,0:T(8,128)(2,1)S(1)}, u32[]{:S(2)}, u32[]{:S(2)}) collective-permute-start(bf16[128,256]{1,0:T(8,128)(2,1)S(1)} %fusion.41), channel_id=1, source_target_pairs={{0,8},{2,10},{4,12},{6,14},{8,0},{10,2},{12,4},{14,6},{1,9},{3,11}... | collective-permute-start | bytes 196616 | tf_op jit(solution)/shard_map/ppermute | solution.py:18
  21.7 2.7 %collective-permute-start.7 = (bf16[128,256]{1,0:T(8,128)(2,1)S(1)}, bf16[128,256]{1,0:T(8,128)(2,1)S(1)}, u32[]{:S(2)}, u32[]{:S(2)}) collective-permute-start(bf16[128,256]{1,0:T(8,128)(2,1)S(1)} %fusion.39), channel_id=1, source_target_pairs={{0,8},{2,10},{4,12},{6,14},{8,0},{10,2},{12,4},{14,6},{1,9},{3,11}... | collective-permute-start | bytes 196616 | tf_op jit(solution)/shard_map/ppermute | solution.py:18
  24.8 2.4 %collective-permute-done.17 = bf16[128,256]{1,0:T(8,128)(2,1)S(1)} collective-permute-done((bf16[128,256]{1,0:T(8,128)(2,1)S(1)}, bf16[128,256]{1,0:T(8,128)(2,1)S(1)}, u32[]{:S(2)}, u32[]{:S(2)}) %collective-permute-start.17) | collective-permute-done | bytes 65568 | tf_op jit(solution)/shard_map/ppermute | solution.py:18
  27.3 2.7 %collective-permute-done.12 = bf16[128,256]{1,0:T(8,128)(2,1)S(1)} collective-permute-done((bf16[128,256]{1,0:T(8,128)(2,1)S(1)}, bf16[128,256]{1,0:T(8,128)(2,1)S(1)}, u32[]{:S(2)}, u32[]{:S(2)}) %collective-permute-start.12) | collective-permute-done | bytes 65568 | tf_op jit(solution)/shard_map/ppermute | solution.py:18
  30.1 0.6 collective-permute-done.7
  30.7 0.6 collective-permute-start.8
  31.4 0.9 %collective-permute-start.3 = (bf16[128,256]{1,0:T(8,128)(2,1)S(1)}, bf16[128,256]{1,0:T(8,128)(2,1)S(1)}, u32[]{:S(2)}, u32[]{:S(2)}) collective-permute-start(bf16[128,256]{1,0:T(8,128)(2,1)S(1)} %multiply_convert_fusion.3), channel_id=1, source_target_pairs={{0,4},{2,6},{4,0},{6,2},{8,12},{10,14},{12,8},{14,10},{1,5},{3,7},... | collective-permute-start | bytes 196616 | tf_op jit(solution)/shard_map/ppermute | solution.py:18
  32.4 1.2 %collective-permute-start.19 = (bf16[128,512]{1,0:T(8,128)(2,1)S(1)}, bf16[128,512]{1,0:T(8,128)(2,1)S(1)}, u32[]{:S(2)}, u32[]{:S(2)}) collective-permute-start(bf16[128,512]{1,0:T(8,128)(2,1)S(1)} %pad_maximum_fusion.4), channel_id=1, source_target_pairs={{0,4},{2,6},{4,0},{6,2},{8,12},{10,14},{12,8},{14,10},{1,5},{3,7},... | collective-permute-start | bytes 393224 | tf_op jit(solution)/shard_map/ppermute | solution.py:18
  33.6 1.4 %collective-permute-done.13 = bf16[128,256]{1,0:T(8,128)(2,1)S(1)} collective-permute-done((bf16[128,256]{1,0:T(8,128)(2,1)S(1)}, bf16[128,256]{1,0:T(8,128)(2,1)S(1)}, u32[]{:S(2)}, u32[]{:S(2)}) %collective-permute-start.13) | collective-permute-done | bytes 65568 | tf_op jit(solution)/shard_map/ppermute | solution.py:18
  35.7 1.4 %collective-permute-start.9 = (bf16[128,512]{1,0:T(8,128)(2,1)S(1)}, bf16[128,512]{1,0:T(8,128)(2,1)S(1)}, u32[]{:S(2)}, u32[]{:S(2)}) collective-permute-start(bf16[128,512]{1,0:T(8,128)(2,1)S(1)} %pad_maximum_fusion.2), channel_id=1, source_target_pairs={{0,4},{2,6},{4,0},{6,2},{8,12},{10,14},{12,8},{14,10},{1,5},{3,7},... | collective-permute-start | bytes 393224 | tf_op jit(solution)/shard_map/ppermute | solution.py:18
  37.1 0.9 %collective-permute-start.4 = (bf16[128,512]{1,0:T(8,128)(2,1)S(1)}, bf16[128,512]{1,0:T(8,128)(2,1)S(1)}, u32[]{:S(2)}, u32[]{:S(2)}) collective-permute-start(bf16[128,512]{1,0:T(8,128)(2,1)S(1)} %pad_maximum_fusion.1), channel_id=1, source_target_pairs={{0,2},{2,0},{4,6},{6,4},{8,10},{10,8},{12,14},{14,12},{1,3},{3,1},... | collective-permute-start | bytes 393224 | tf_op jit(solution)/shard_map/ppermute | solution.py:18
  38.0 1.1 %collective-permute-done.19 = bf16[128,512]{1,0:T(8,128)(2,1)S(1)} collective-permute-done((bf16[128,512]{1,0:T(8,128)(2,1)S(1)}, bf16[128,512]{1,0:T(8,128)(2,1)S(1)}, u32[]{:S(2)}, u32[]{:S(2)}) %collective-permute-start.19) | collective-permute-done | bytes 131104 | tf_op jit(solution)/shard_map/ppermute | solution.py:18
  41.2 1.0 %collective-permute-done.4 = bf16[128,512]{1,0:T(8,128)(2,1)S(1)} collective-permute-done((bf16[128,512]{1,0:T(8,128)(2,1)S(1)}, bf16[128,512]{1,0:T(8,128)(2,1)S(1)}, u32[]{:S(2)}, u32[]{:S(2)}) %collective-permute-start.4) | collective-permute-done | bytes 131104 | tf_op jit(solution)/shard_map/ppermute | solution.py:18
  42.7 1.5 %collective-permute-done.20.other_ref = f32[512,128]{1,0:T(8,128)S(1)} collective-permute-done((f32[512,128]{1,0:T(8,128)S(1)}, f32[512,128]{1,0:T(8,128)S(1)}, u32[]{:S(2)}, u32[]{:S(2)}) %collective-permute-start.20) | collective-permute-done | bytes 262176 | tf_op jit(solution)/shard_map/ppermute | solution.py:18
  44.7 2.3 %collective-permute-start.24 = (f32[72,128]{1,0:T(8,128)S(1)}, f32[72,128]{1,0:T(8,128)S(1)}, u32[]{:S(2)}, u32[]{:S(2)}) collective-permute-start(f32[72,128]{1,0:T(8,128)S(1)} %make_gram.1), channel_id=1, source_target_pairs={{0,10},{1,15},{2,8},{3,13},{4,14},{5,11},{6,12},{7,9},{8,2},{9,7},... | collective-permute-start | bytes 110600 | tf_op jit(solution)/shard_map/ppermute | solution.py:36
  47.0 1.0 %collective-permute-start.23 = (f32[72,128]{1,0:T(8,128)S(1)}, f32[72,128]{1,0:T(8,128)S(1)}, u32[]{:S(2)}, u32[]{:S(2)}) collective-permute-start(f32[72,128]{1,0:T(8,128)S(1)} %make_gram.1), channel_id=1, source_target_pairs={{0,8},{1,13},{2,10},{3,15},{4,12},{5,9},{6,14},{7,11},{8,0},{9,5},... | collective-permute-start | bytes 110600 | tf_op jit(solution)/shard_map/ppermute | solution.py:36
  48.0 1.2 %collective-permute-start.22 = (f32[72,128]{1,0:T(8,128)S(1)}, f32[72,128]{1,0:T(8,128)S(1)}, u32[]{:S(2)}, u32[]{:S(2)}) collective-permute-start(f32[72,128]{1,0:T(8,128)S(1)} %make_gram.1), channel_id=1, source_target_pairs={{0,2},{1,7},{2,0},{3,5},{4,6},{5,3},{6,4},{7,1},{8,10},{9,15},{10,... | collective-permute-start | bytes 110600 | tf_op jit(solution)/shard_map/ppermute | solution.py:36
  49.2 0.7 collective-permute-start.21
  49.9 1.5 %collective-permute-done.24 = f32[72,128]{1,0:T(8,128)S(1)} collective-permute-done((f32[72,128]{1,0:T(8,128)S(1)}, f32[72,128]{1,0:T(8,128)S(1)}, u32[]{:S(2)}, u32[]{:S(2)}) %collective-permute-start.24) | collective-permute-done | bytes 36896 | tf_op jit(solution)/shard_map/ppermute | solution.py:36
  51.4 1.2 %collective-permute-done.23 = f32[72,128]{1,0:T(8,128)S(1)} collective-permute-done((f32[72,128]{1,0:T(8,128)S(1)}, f32[72,128]{1,0:T(8,128)S(1)}, u32[]{:S(2)}, u32[]{:S(2)}) %collective-permute-start.23) | collective-permute-done | bytes 36896 | tf_op jit(solution)/shard_map/ppermute | solution.py:36
  52.5 1.4 %collective-permute-start.25 = (f32[72,128]{1,0:T(8,128)S(1)}, f32[72,128]{1,0:T(8,128)S(1)}, u32[]{:S(2)}, u32[]{:S(2)}) collective-permute-start(f32[72,128]{1,0:T(8,128)S(1)} %add_add_fusion), channel_id=1, source_target_pairs={{0,1},{1,0},{2,3},{3,2},{4,5},{5,4},{6,7},{7,6},{8,9},{9,8},{10,11... | collective-permute-start | bytes 110600 | tf_op jit(solution)/shard_map/ppermute | solution.py:18
  53.9 0.9 %collective-permute-done.25 = f32[72,128]{1,0:T(8,128)S(1)} collective-permute-done((f32[72,128]{1,0:T(8,128)S(1)}, f32[72,128]{1,0:T(8,128)S(1)}, u32[]{:S(2)}, u32[]{:S(2)}) %collective-permute-start.25) | collective-permute-done | bytes 36896 | tf_op jit(solution)/shard_map/ppermute | solution.py:18
  54.8 4.6 %make_basis.1 = (f32[512,128]{1,0:T(8,128)}, f32[128,1024]{1,0:T(8,128)S(1)}, f32[128,1024]{1,0:T(8,128)S(1)}, f32[128,1024]{1,0:T(8,128)S(1)}, f32[128,1024]{1,0:T(8,128)S(1)}) custom-call(f32[72,128]{1,0:T(8,128)S(1)} %add.116.gram_ref, f32[512,128]{1,0:T(8,128)S(1)} %fusion.2.mine_ref, f32[512,128]{1,0:T(8,128)S(1)} %collective-permute-done.20.other_ref, ...), custom_call_target="tpu_custom_call" | custom-call | tf_op jit(solution)/shard_map/make_basis/pallas_call | solution.py:277
  59.5 0.9 %collective-permute-start.26 = (bf16[2,2,16,1024]{3,2,0,1:T(8,128)(2,1)S(1)}, bf16[2,2,16,1024]{3,2,0,1:T(8,128)(2,1)S(1)}, u32[]{:S(2)}, u32[]{:S(2)}) collective-permute-start(bf16[2,2,16,1024]{3,2,0,1:T(8,128)(2,1)S(1)} %fusion.22), channel_id=1, source_target_pairs={{0,2},{2,0},{4,6},{6,4},{8,10},{10,8},{12,14},{14,12},{1,3},{3,1},... | collective-permute-start | bytes 393224 | tf_op jit(solution)/shard_map/ppermute | solution.py:18
  60.4 1.8 %collective-permute-start.29 = (bf16[2,2,16,1024]{3,2,0,1:T(8,128)(2,1)S(1)}, bf16[2,2,16,1024]{3,2,0,1:T(8,128)(2,1)S(1)}, u32[]{:S(2)}, u32[]{:S(2)}) collective-permute-start(bf16[2,2,16,1024]{3,2,0,1:T(8,128)(2,1)S(1)} %fusion.23), channel_id=1, source_target_pairs={{0,4},{2,6},{4,0},{6,2},{8,12},{10,14},{12,8},{14,10},{1,5},{3,7},... | collective-permute-start | bytes 393224 | tf_op jit(solution)/shard_map/ppermute | solution.py:18
  62.3 1.3 %collective-permute-start.32 = (bf16[2,2,16,1024]{3,2,0,1:T(8,128)(2,1)S(1)}, bf16[2,2,16,1024]{3,2,0,1:T(8,128)(2,1)S(1)}, u32[]{:S(2)}, u32[]{:S(2)}) collective-permute-start(bf16[2,2,16,1024]{3,2,0,1:T(8,128)(2,1)S(1)} %fusion.24), channel_id=1, source_target_pairs={{0,2},{2,0},{4,6},{6,4},{8,10},{10,8},{12,14},{14,12},{1,3},{3,1},... | collective-permute-start | bytes 393224 | tf_op jit(solution)/shard_map/ppermute | solution.py:18
  64.0 1.8 %collective-permute-done.26 = bf16[2,2,16,1024]{3,2,0,1:T(8,128)(2,1)S(1)} collective-permute-done((bf16[2,2,16,1024]{3,2,0,1:T(8,128)(2,1)S(1)}, bf16[2,2,16,1024]{3,2,0,1:T(8,128)(2,1)S(1)}, u32[]{:S(2)}, u32[]{:S(2)}) %collective-permute-start.26) | collective-permute-done | bytes 131104 | tf_op jit(solution)/shard_map/ppermute | solution.py:18
  65.8 1.9 %collective-permute-start.27 = (bf16[2,16,1024]{2,1,0:T(8,128)(2,1)S(1)}, bf16[2,16,1024]{2,1,0:T(8,128)(2,1)S(1)}, u32[]{:S(2)}, u32[]{:S(2)}) collective-permute-start(bf16[2,16,1024]{2,1,0:T(8,128)(2,1)S(1)} %fusion.26), channel_id=1, source_target_pairs={{0,4},{2,6},{4,0},{6,2},{8,12},{10,14},{12,8},{14,10},{1,5},{3,7},... | collective-permute-start | bytes 196616 | tf_op jit(solution)/shard_map/ppermute | solution.py:18
  67.8 0.9 %collective-permute-start.30 = (bf16[2,16,1024]{2,1,0:T(8,128)(2,1)S(1)}, bf16[2,16,1024]{2,1,0:T(8,128)(2,1)S(1)}, u32[]{:S(2)}, u32[]{:S(2)}) collective-permute-start(bf16[2,16,1024]{2,1,0:T(8,128)(2,1)S(1)} %fusion.27), channel_id=1, source_target_pairs={{0,2},{2,0},{4,6},{6,4},{8,10},{10,8},{12,14},{14,12},{1,3},{3,1},... | collective-permute-start | bytes 196616 | tf_op jit(solution)/shard_map/ppermute | solution.py:18
  68.8 1.4 %collective-permute-start.33 = (bf16[2,16,1024]{2,1,0:T(8,128)(2,1)S(1)}, bf16[2,16,1024]{2,1,0:T(8,128)(2,1)S(1)}, u32[]{:S(2)}, u32[]{:S(2)}) collective-permute-start(bf16[2,16,1024]{2,1,0:T(8,128)(2,1)S(1)} %fusion.28), channel_id=1, source_target_pairs={{0,4},{2,6},{4,0},{6,2},{8,12},{10,14},{12,8},{14,10},{1,5},{3,7},... | collective-permute-start | bytes 196616 | tf_op jit(solution)/shard_map/ppermute | solution.py:18
  70.2 0.8 %collective-permute-start.36 = (bf16[2,16,1024]{2,1,0:T(8,128)(2,1)S(1)}, bf16[2,16,1024]{2,1,0:T(8,128)(2,1)S(1)}, u32[]{:S(2)}, u32[]{:S(2)}) collective-permute-start(bf16[2,16,1024]{2,1,0:T(8,128)(2,1)S(1)} %fusion.29), channel_id=1, source_target_pairs={{0,2},{2,0},{4,6},{6,4},{8,10},{10,8},{12,14},{14,12},{1,3},{3,1},... | collective-permute-start | bytes 196616 | tf_op jit(solution)/shard_map/ppermute | solution.py:18
  71.1 1.8 %collective-permute-start.28 = (bf16[16,1024]{1,0:T(8,128)(2,1)S(1)}, bf16[16,1024]{1,0:T(8,128)(2,1)S(1)}, u32[]{:S(2)}, u32[]{:S(2)}) collective-permute-start(bf16[16,1024]{1,0:T(8,128)(2,1)S(1)} %fusion.34), channel_id=1, source_target_pairs={{0,8},{2,10},{4,12},{6,14},{8,0},{10,2},{12,4},{14,6},{1,9},{3,11}... | collective-permute-start | bytes 98312 | tf_op jit(solution)/shard_map/ppermute | solution.py:18
  72.9 1.2 %collective-permute-start.31 = (bf16[16,1024]{1,0:T(8,128)(2,1)S(1)}, bf16[16,1024]{1,0:T(8,128)(2,1)S(1)}, u32[]{:S(2)}, u32[]{:S(2)}) collective-permute-start(bf16[16,1024]{1,0:T(8,128)(2,1)S(1)} %fusion.35), channel_id=1, source_target_pairs={{0,8},{2,10},{4,12},{6,14},{8,0},{10,2},{12,4},{14,6},{1,9},{3,11}... | collective-permute-start | bytes 98312 | tf_op jit(solution)/shard_map/ppermute | solution.py:18
  74.2 1.8 %collective-permute-start.34 = (bf16[16,1024]{1,0:T(8,128)(2,1)S(1)}, bf16[16,1024]{1,0:T(8,128)(2,1)S(1)}, u32[]{:S(2)}, u32[]{:S(2)}) collective-permute-start(bf16[16,1024]{1,0:T(8,128)(2,1)S(1)} %fusion.36), channel_id=1, source_target_pairs={{0,8},{2,10},{4,12},{6,14},{8,0},{10,2},{12,4},{14,6},{1,9},{3,11}... | collective-permute-start | bytes 98312 | tf_op jit(solution)/shard_map/ppermute | solution.py:18
  76.1 1.2 %collective-permute-start.37 = (bf16[16,1024]{1,0:T(8,128)(2,1)S(1)}, bf16[16,1024]{1,0:T(8,128)(2,1)S(1)}, u32[]{:S(2)}, u32[]{:S(2)}) collective-permute-start(bf16[16,1024]{1,0:T(8,128)(2,1)S(1)} %fusion.37), channel_id=1, source_target_pairs={{0,8},{2,10},{4,12},{6,14},{8,0},{10,2},{12,4},{14,6},{1,9},{3,11}... | collective-permute-start | bytes 98312 | tf_op jit(solution)/shard_map/ppermute | solution.py:18
  77.3 1.3 %collective-permute-done.31 = bf16[16,1024]{1,0:T(8,128)(2,1)S(1)} collective-permute-done((bf16[16,1024]{1,0:T(8,128)(2,1)S(1)}, bf16[16,1024]{1,0:T(8,128)(2,1)S(1)}, u32[]{:S(2)}, u32[]{:S(2)}) %collective-permute-start.31) | collective-permute-done | bytes 32800 | tf_op jit(solution)/shard_map/ppermute | solution.py:18
  79.2 1.7 %collective-permute-done.37 = bf16[16,1024]{1,0:T(8,128)(2,1)S(1)} collective-permute-done((bf16[16,1024]{1,0:T(8,128)(2,1)S(1)}, bf16[16,1024]{1,0:T(8,128)(2,1)S(1)}, u32[]{:S(2)}, u32[]{:S(2)}) %collective-permute-start.37) | collective-permute-done | bytes 32800 | tf_op jit(solution)/shard_map/ppermute | solution.py:18
  81.0 0.7 pad_maximum_fusion
  (105 shorter events, 7.8 us)
Async XLA Ops:
  0.6 0.9 %copy-start = (bf16[512,128]{1,0:T(8,128)(2,1)S(1)}, bf16[512,128]{1,0:T(8,128)(2,1)}, u32[]{:S(2)}) copy-start(bf16[512,128]{1,0:T(8,128)(2,1)} %start_ref.3) | copy-start | bytes 393220
  1.6 6.8 %copy-start.1 = (bf16[512,128]{1,0:T(8,128)(2,1)S(1)}, bf16[512,128]{1,0:T(8,128)(2,1)}, u32[]{:S(2)}) copy-start(bf16[512,128]{1,0:T(8,128)(2,1)} %start_ref.3) | copy-start | bytes 393220
  3.6 7.5 %collective-permute-start.15 = (bf16[128,512]{1,0:T(8,128)(2,1)S(1)}, bf16[128,512]{1,0:T(8,128)(2,1)S(1)}, u32[]{:S(2)}, u32[]{:S(2)}) collective-permute-start(bf16[128,512]{1,0:T(8,128)(2,1)S(1)} %select_convert_fusion.4), channel_id=1, source_target_pairs={{0,4},{2,6},{4,0},{6,2},{8,12},{10,14},{12,8},{14,10},{1,5},{3,7},... | collective-permute-start | bytes 393224 | tf_op jit(solution)/shard_map/ppermute | solution.py:18
  6.8 6.4 %collective-permute-start.10 = (bf16[128,512]{1,0:T(8,128)(2,1)S(1)}, bf16[128,512]{1,0:T(8,128)(2,1)S(1)}, u32[]{:S(2)}, u32[]{:S(2)}) collective-permute-start(bf16[128,512]{1,0:T(8,128)(2,1)S(1)} %select_convert_fusion.5), channel_id=1, source_target_pairs={{0,2},{2,0},{4,6},{6,4},{8,10},{10,8},{12,14},{14,12},{1,3},{3,1},... | collective-permute-start | bytes 393224 | tf_op jit(solution)/shard_map/ppermute | solution.py:18
  10.4 5.7 %collective-permute-start.5 = (bf16[128,512]{1,0:T(8,128)(2,1)S(1)}, bf16[128,512]{1,0:T(8,128)(2,1)S(1)}, u32[]{:S(2)}, u32[]{:S(2)}) collective-permute-start(bf16[128,512]{1,0:T(8,128)(2,1)S(1)} %select_convert_fusion.6), channel_id=1, source_target_pairs={{0,4},{2,6},{4,0},{6,2},{8,12},{10,14},{12,8},{14,10},{1,5},{3,7},... | collective-permute-start | bytes 393224 | tf_op jit(solution)/shard_map/ppermute | solution.py:18
  10.9 5.9 %collective-permute-start = (bf16[128,512]{1,0:T(8,128)(2,1)S(1)}, bf16[128,512]{1,0:T(8,128)(2,1)S(1)}, u32[]{:S(2)}, u32[]{:S(2)}) collective-permute-start(bf16[128,512]{1,0:T(8,128)(2,1)S(1)} %select_convert_fusion.7), channel_id=1, source_target_pairs={{0,2},{2,0},{4,6},{6,4},{8,10},{10,8},{12,14},{14,12},{1,3},{3,1},... | collective-permute-start | bytes 393224 | tf_op jit(solution)/shard_map/ppermute | solution.py:18
  11.2 7.3 %collective-permute-start.16 = (bf16[128,256]{1,0:T(8,128)(2,1)S(1)}, bf16[128,256]{1,0:T(8,128)(2,1)S(1)}, u32[]{:S(2)}, u32[]{:S(2)}) collective-permute-start(bf16[128,256]{1,0:T(8,128)(2,1)S(1)} %select_convert_fusion.12), channel_id=1, source_target_pairs={{0,2},{2,0},{4,6},{6,4},{8,10},{10,8},{12,14},{14,12},{1,3},{3,1},... | collective-permute-start | bytes 196616 | tf_op jit(solution)/shard_map/ppermute | solution.py:18
  13.2 25.9 %copy-start.2 = (bf16[512,4096]{1,0:T(8,128)(2,1)S(1)}, bf16[512,4096]{1,0:T(8,128)(2,1)}, u32[]{:S(2)}) copy-start(bf16[512,4096]{1,0:T(8,128)(2,1)} %slab_ref.5) | copy-start | bytes 12582916
  13.3 8.0 %collective-permute-start.11 = (bf16[128,256]{1,0:T(8,128)(2,1)S(1)}, bf16[128,256]{1,0:T(8,128)(2,1)S(1)}, u32[]{:S(2)}, u32[]{:S(2)}) collective-permute-start(bf16[128,256]{1,0:T(8,128)(2,1)S(1)} %select_convert_fusion.13), channel_id=1, source_target_pairs={{0,4},{2,6},{4,0},{6,2},{8,12},{10,14},{12,8},{14,10},{1,5},{3,7},... | collective-permute-start | bytes 196616 | tf_op jit(solution)/shard_map/ppermute | solution.py:18
  16.2 5.4 %collective-permute-start.6 = (bf16[128,256]{1,0:T(8,128)(2,1)S(1)}, bf16[128,256]{1,0:T(8,128)(2,1)S(1)}, u32[]{:S(2)}, u32[]{:S(2)}) collective-permute-start(bf16[128,256]{1,0:T(8,128)(2,1)S(1)} %select_convert_fusion.14), channel_id=1, source_target_pairs={{0,2},{2,0},{4,6},{6,4},{8,10},{10,8},{12,14},{14,12},{1,3},{3,1},... | collective-permute-start | bytes 196616 | tf_op jit(solution)/shard_map/ppermute | solution.py:18
  16.9 7.5 %collective-permute-start.1 = (bf16[128,256]{1,0:T(8,128)(2,1)S(1)}, bf16[128,256]{1,0:T(8,128)(2,1)S(1)}, u32[]{:S(2)}, u32[]{:S(2)}) collective-permute-start(bf16[128,256]{1,0:T(8,128)(2,1)S(1)} %select_convert_fusion.15), channel_id=1, source_target_pairs={{0,4},{2,6},{4,0},{6,2},{8,12},{10,14},{12,8},{14,10},{1,5},{3,7},... | collective-permute-start | bytes 196616 | tf_op jit(solution)/shard_map/ppermute | solution.py:18
  18.5 8.6 %collective-permute-start.17 = (bf16[128,256]{1,0:T(8,128)(2,1)S(1)}, bf16[128,256]{1,0:T(8,128)(2,1)S(1)}, u32[]{:S(2)}, u32[]{:S(2)}) collective-permute-start(bf16[128,256]{1,0:T(8,128)(2,1)S(1)} %fusion.41), channel_id=1, source_target_pairs={{0,8},{2,10},{4,12},{6,14},{8,0},{10,2},{12,4},{14,6},{1,9},{3,11}... | collective-permute-start | bytes 196616 | tf_op jit(solution)/shard_map/ppermute | solution.py:18
  21.2 8.7 %collective-permute-start.12 = (bf16[128,256]{1,0:T(8,128)(2,1)S(1)}, bf16[128,256]{1,0:T(8,128)(2,1)S(1)}, u32[]{:S(2)}, u32[]{:S(2)}) collective-permute-start(bf16[128,256]{1,0:T(8,128)(2,1)S(1)} %fusion.40), channel_id=1, source_target_pairs={{0,8},{2,10},{4,12},{6,14},{8,0},{10,2},{12,4},{14,6},{1,9},{3,11}... | collective-permute-start | bytes 196616 | tf_op jit(solution)/shard_map/ppermute | solution.py:18
  21.7 9.0 %collective-permute-start.7 = (bf16[128,256]{1,0:T(8,128)(2,1)S(1)}, bf16[128,256]{1,0:T(8,128)(2,1)S(1)}, u32[]{:S(2)}, u32[]{:S(2)}) collective-permute-start(bf16[128,256]{1,0:T(8,128)(2,1)S(1)} %fusion.39), channel_id=1, source_target_pairs={{0,8},{2,10},{4,12},{6,14},{8,0},{10,2},{12,4},{14,6},{1,9},{3,11}... | collective-permute-start | bytes 196616 | tf_op jit(solution)/shard_map/ppermute | solution.py:18
  24.4 7.0 %collective-permute-start.2 = (bf16[128,256]{1,0:T(8,128)(2,1)S(1)}, bf16[128,256]{1,0:T(8,128)(2,1)S(1)}, u32[]{:S(2)}, u32[]{:S(2)}) collective-permute-start(bf16[128,256]{1,0:T(8,128)(2,1)S(1)} %fusion.38), channel_id=1, source_target_pairs={{0,8},{2,10},{4,12},{6,14},{8,0},{10,2},{12,4},{14,6},{1,9},{3,11}... | collective-permute-start | bytes 196616 | tf_op jit(solution)/shard_map/ppermute | solution.py:18
  27.2 5.2 %collective-permute-start.18 = (bf16[128,256]{1,0:T(8,128)(2,1)S(1)}, bf16[128,256]{1,0:T(8,128)(2,1)S(1)}, u32[]{:S(2)}, u32[]{:S(2)}) collective-permute-start(bf16[128,256]{1,0:T(8,128)(2,1)S(1)} %multiply_convert_fusion), channel_id=1, source_target_pairs={{0,2},{2,0},{4,6},{6,4},{8,10},{10,8},{12,14},{14,12},{1,3},{3,1},... | collective-permute-start | bytes 196616 | tf_op jit(solution)/shard_map/ppermute | solution.py:18
  30.0 5.0 %collective-permute-start.13 = (bf16[128,256]{1,0:T(8,128)(2,1)S(1)}, bf16[128,256]{1,0:T(8,128)(2,1)S(1)}, u32[]{:S(2)}, u32[]{:S(2)}) collective-permute-start(bf16[128,256]{1,0:T(8,128)(2,1)S(1)} %multiply_convert_fusion.1), channel_id=1, source_target_pairs={{0,4},{2,6},{4,0},{6,2},{8,12},{10,14},{12,8},{14,10},{1,5},{3,7},... | collective-permute-start | bytes 196616 | tf_op jit(solution)/shard_map/ppermute | solution.py:18
  30.7 4.9 %collective-permute-start.8 = (bf16[128,256]{1,0:T(8,128)(2,1)S(1)}, bf16[128,256]{1,0:T(8,128)(2,1)S(1)}, u32[]{:S(2)}, u32[]{:S(2)}) collective-permute-start(bf16[128,256]{1,0:T(8,128)(2,1)S(1)} %multiply_convert_fusion.2), channel_id=1, source_target_pairs={{0,2},{2,0},{4,6},{6,4},{8,10},{10,8},{12,14},{14,12},{1,3},{3,1},... | collective-permute-start | bytes 196616 | tf_op jit(solution)/shard_map/ppermute | solution.py:18
  31.4 5.7 %collective-permute-start.3 = (bf16[128,256]{1,0:T(8,128)(2,1)S(1)}, bf16[128,256]{1,0:T(8,128)(2,1)S(1)}, u32[]{:S(2)}, u32[]{:S(2)}) collective-permute-start(bf16[128,256]{1,0:T(8,128)(2,1)S(1)} %multiply_convert_fusion.3), channel_id=1, source_target_pairs={{0,4},{2,6},{4,0},{6,2},{8,12},{10,14},{12,8},{14,10},{1,5},{3,7},... | collective-permute-start | bytes 196616 | tf_op jit(solution)/shard_map/ppermute | solution.py:18
  32.4 6.7 %collective-permute-start.19 = (bf16[128,512]{1,0:T(8,128)(2,1)S(1)}, bf16[128,512]{1,0:T(8,128)(2,1)S(1)}, u32[]{:S(2)}, u32[]{:S(2)}) collective-permute-start(bf16[128,512]{1,0:T(8,128)(2,1)S(1)} %pad_maximum_fusion.4), channel_id=1, source_target_pairs={{0,4},{2,6},{4,0},{6,2},{8,12},{10,14},{12,8},{14,10},{1,5},{3,7},... | collective-permute-start | bytes 393224 | tf_op jit(solution)/shard_map/ppermute | solution.py:18
  35.0 5.0 %collective-permute-start.14 = (bf16[128,512]{1,0:T(8,128)(2,1)S(1)}, bf16[128,512]{1,0:T(8,128)(2,1)S(1)}, u32[]{:S(2)}, u32[]{:S(2)}) collective-permute-start(bf16[128,512]{1,0:T(8,128)(2,1)S(1)} %pad_maximum_fusion.3), channel_id=1, source_target_pairs={{0,2},{2,0},{4,6},{6,4},{8,10},{10,8},{12,14},{14,12},{1,3},{3,1},... | collective-permute-start | bytes 393224 | tf_op jit(solution)/shard_map/ppermute | solution.py:18
  35.7 5.0 %collective-permute-start.9 = (bf16[128,512]{1,0:T(8,128)(2,1)S(1)}, bf16[128,512]{1,0:T(8,128)(2,1)S(1)}, u32[]{:S(2)}, u32[]{:S(2)}) collective-permute-start(bf16[128,512]{1,0:T(8,128)(2,1)S(1)} %pad_maximum_fusion.2), channel_id=1, source_target_pairs={{0,4},{2,6},{4,0},{6,2},{8,12},{10,14},{12,8},{14,10},{1,5},{3,7},... | collective-permute-start | bytes 393224 | tf_op jit(solution)/shard_map/ppermute | solution.py:18
  37.1 5.0 %collective-permute-start.4 = (bf16[128,512]{1,0:T(8,128)(2,1)S(1)}, bf16[128,512]{1,0:T(8,128)(2,1)S(1)}, u32[]{:S(2)}, u32[]{:S(2)}) collective-permute-start(bf16[128,512]{1,0:T(8,128)(2,1)S(1)} %pad_maximum_fusion.1), channel_id=1, source_target_pairs={{0,2},{2,0},{4,6},{6,4},{8,10},{10,8},{12,14},{14,12},{1,3},{3,1},... | collective-permute-start | bytes 393224 | tf_op jit(solution)/shard_map/ppermute | solution.py:18
  42.6 1.6 %collective-permute-start.20 = (f32[512,128]{1,0:T(8,128)S(1)}, f32[512,128]{1,0:T(8,128)S(1)}, u32[]{:S(2)}, u32[]{:S(2)}) collective-permute-start(f32[512,128]{1,0:T(8,128)S(1)} %fusion.2.mine_ref), channel_id=1, source_target_pairs={{0,1},{1,0},{2,3},{3,2},{4,5},{5,4},{6,7},{7,6},{8,9},{9,8},{10,11... | collective-permute-start | bytes 786440 | tf_op jit(solution)/shard_map/ppermute | solution.py:18
  44.7 6.6 %collective-permute-start.24 = (f32[72,128]{1,0:T(8,128)S(1)}, f32[72,128]{1,0:T(8,128)S(1)}, u32[]{:S(2)}, u32[]{:S(2)}) collective-permute-start(f32[72,128]{1,0:T(8,128)S(1)} %make_gram.1), channel_id=1, source_target_pairs={{0,10},{1,15},{2,8},{3,13},{4,14},{5,11},{6,12},{7,9},{8,2},{9,7},... | collective-permute-start | bytes 110600 | tf_op jit(solution)/shard_map/ppermute | solution.py:36
  47.0 5.5 %collective-permute-start.23 = (f32[72,128]{1,0:T(8,128)S(1)}, f32[72,128]{1,0:T(8,128)S(1)}, u32[]{:S(2)}, u32[]{:S(2)}) collective-permute-start(f32[72,128]{1,0:T(8,128)S(1)} %make_gram.1), channel_id=1, source_target_pairs={{0,8},{1,13},{2,10},{3,15},{4,12},{5,9},{6,14},{7,11},{8,0},{9,5},... | collective-permute-start | bytes 110600 | tf_op jit(solution)/shard_map/ppermute | solution.py:36
  48.0 4.5 %collective-permute-start.22 = (f32[72,128]{1,0:T(8,128)S(1)}, f32[72,128]{1,0:T(8,128)S(1)}, u32[]{:S(2)}, u32[]{:S(2)}) collective-permute-start(f32[72,128]{1,0:T(8,128)S(1)} %make_gram.1), channel_id=1, source_target_pairs={{0,2},{1,7},{2,0},{3,5},{4,6},{5,3},{6,4},{7,1},{8,10},{9,15},{10,... | collective-permute-start | bytes 110600 | tf_op jit(solution)/shard_map/ppermute | solution.py:36
  49.2 3.3 %collective-permute-start.21 = (f32[72,128]{1,0:T(8,128)S(1)}, f32[72,128]{1,0:T(8,128)S(1)}, u32[]{:S(2)}, u32[]{:S(2)}) collective-permute-start(f32[72,128]{1,0:T(8,128)S(1)} %make_gram.1), channel_id=1, source_target_pairs={{1,5},{3,7},{5,1},{7,3},{9,13},{11,15},{13,9},{15,11},{17,21},{19,... | collective-permute-start | bytes 110600 | tf_op jit(solution)/shard_map/ppermute | solution.py:36
  52.5 2.2 %collective-permute-start.25 = (f32[72,128]{1,0:T(8,128)S(1)}, f32[72,128]{1,0:T(8,128)S(1)}, u32[]{:S(2)}, u32[]{:S(2)}) collective-permute-start(f32[72,128]{1,0:T(8,128)S(1)} %add_add_fusion), channel_id=1, source_target_pairs={{0,1},{1,0},{2,3},{3,2},{4,5},{5,4},{6,7},{7,6},{8,9},{9,8},{10,11... | collective-permute-start | bytes 110600 | tf_op jit(solution)/shard_map/ppermute | solution.py:18
  59.5 6.3 %collective-permute-start.26 = (bf16[2,2,16,1024]{3,2,0,1:T(8,128)(2,1)S(1)}, bf16[2,2,16,1024]{3,2,0,1:T(8,128)(2,1)S(1)}, u32[]{:S(2)}, u32[]{:S(2)}) collective-permute-start(bf16[2,2,16,1024]{3,2,0,1:T(8,128)(2,1)S(1)} %fusion.22), channel_id=1, source_target_pairs={{0,2},{2,0},{4,6},{6,4},{8,10},{10,8},{12,14},{14,12},{1,3},{3,1},... | collective-permute-start | bytes 393224 | tf_op jit(solution)/shard_map/ppermute | solution.py:18
  60.4 7.3 %collective-permute-start.29 = (bf16[2,2,16,1024]{3,2,0,1:T(8,128)(2,1)S(1)}, bf16[2,2,16,1024]{3,2,0,1:T(8,128)(2,1)S(1)}, u32[]{:S(2)}, u32[]{:S(2)}) collective-permute-start(bf16[2,2,16,1024]{3,2,0,1:T(8,128)(2,1)S(1)} %fusion.23), channel_id=1, source_target_pairs={{0,4},{2,6},{4,0},{6,2},{8,12},{10,14},{12,8},{14,10},{1,5},{3,7},... | collective-permute-start | bytes 393224 | tf_op jit(solution)/shard_map/ppermute | solution.py:18
  62.3 6.4 %collective-permute-start.32 = (bf16[2,2,16,1024]{3,2,0,1:T(8,128)(2,1)S(1)}, bf16[2,2,16,1024]{3,2,0,1:T(8,128)(2,1)S(1)}, u32[]{:S(2)}, u32[]{:S(2)}) collective-permute-start(bf16[2,2,16,1024]{3,2,0,1:T(8,128)(2,1)S(1)} %fusion.24), channel_id=1, source_target_pairs={{0,2},{2,0},{4,6},{6,4},{8,10},{10,8},{12,14},{14,12},{1,3},{3,1},... | collective-permute-start | bytes 393224 | tf_op jit(solution)/shard_map/ppermute | solution.py:18
  63.7 6.4 %collective-permute-start.35 = (bf16[2,2,16,1024]{3,2,0,1:T(8,128)(2,1)S(1)}, bf16[2,2,16,1024]{3,2,0,1:T(8,128)(2,1)S(1)}, u32[]{:S(2)}, u32[]{:S(2)}) collective-permute-start(bf16[2,2,16,1024]{3,2,0,1:T(8,128)(2,1)S(1)} %fusion.25), channel_id=1, source_target_pairs={{0,4},{2,6},{4,0},{6,2},{8,12},{10,14},{12,8},{14,10},{1,5},{3,7},... | collective-permute-start | bytes 393224 | tf_op jit(solution)/shard_map/ppermute | solution.py:18
  65.8 5.2 %collective-permute-start.27 = (bf16[2,16,1024]{2,1,0:T(8,128)(2,1)S(1)}, bf16[2,16,1024]{2,1,0:T(8,128)(2,1)S(1)}, u32[]{:S(2)}, u32[]{:S(2)}) collective-permute-start(bf16[2,16,1024]{2,1,0:T(8,128)(2,1)S(1)} %fusion.26), channel_id=1, source_target_pairs={{0,4},{2,6},{4,0},{6,2},{8,12},{10,14},{12,8},{14,10},{1,5},{3,7},... | collective-permute-start | bytes 196616 | tf_op jit(solution)/shard_map/ppermute | solution.py:18
  67.8 5.1 %collective-permute-start.30 = (bf16[2,16,1024]{2,1,0:T(8,128)(2,1)S(1)}, bf16[2,16,1024]{2,1,0:T(8,128)(2,1)S(1)}, u32[]{:S(2)}, u32[]{:S(2)}) collective-permute-start(bf16[2,16,1024]{2,1,0:T(8,128)(2,1)S(1)} %fusion.27), channel_id=1, source_target_pairs={{0,2},{2,0},{4,6},{6,4},{8,10},{10,8},{12,14},{14,12},{1,3},{3,1},... | collective-permute-start | bytes 196616 | tf_op jit(solution)/shard_map/ppermute | solution.py:18
  68.8 5.4 %collective-permute-start.33 = (bf16[2,16,1024]{2,1,0:T(8,128)(2,1)S(1)}, bf16[2,16,1024]{2,1,0:T(8,128)(2,1)S(1)}, u32[]{:S(2)}, u32[]{:S(2)}) collective-permute-start(bf16[2,16,1024]{2,1,0:T(8,128)(2,1)S(1)} %fusion.28), channel_id=1, source_target_pairs={{0,4},{2,6},{4,0},{6,2},{8,12},{10,14},{12,8},{14,10},{1,5},{3,7},... | collective-permute-start | bytes 196616 | tf_op jit(solution)/shard_map/ppermute | solution.py:18
  70.2 5.9 %collective-permute-start.36 = (bf16[2,16,1024]{2,1,0:T(8,128)(2,1)S(1)}, bf16[2,16,1024]{2,1,0:T(8,128)(2,1)S(1)}, u32[]{:S(2)}, u32[]{:S(2)}) collective-permute-start(bf16[2,16,1024]{2,1,0:T(8,128)(2,1)S(1)} %fusion.29), channel_id=1, source_target_pairs={{0,2},{2,0},{4,6},{6,4},{8,10},{10,8},{12,14},{14,12},{1,3},{3,1},... | collective-permute-start | bytes 196616 | tf_op jit(solution)/shard_map/ppermute | solution.py:18
  71.1 6.3 %collective-permute-start.28 = (bf16[16,1024]{1,0:T(8,128)(2,1)S(1)}, bf16[16,1024]{1,0:T(8,128)(2,1)S(1)}, u32[]{:S(2)}, u32[]{:S(2)}) collective-permute-start(bf16[16,1024]{1,0:T(8,128)(2,1)S(1)} %fusion.34), channel_id=1, source_target_pairs={{0,8},{2,10},{4,12},{6,14},{8,0},{10,2},{12,4},{14,6},{1,9},{3,11}... | collective-permute-start | bytes 98312 | tf_op jit(solution)/shard_map/ppermute | solution.py:18
  72.9 5.7 %collective-permute-start.31 = (bf16[16,1024]{1,0:T(8,128)(2,1)S(1)}, bf16[16,1024]{1,0:T(8,128)(2,1)S(1)}, u32[]{:S(2)}, u32[]{:S(2)}) collective-permute-start(bf16[16,1024]{1,0:T(8,128)(2,1)S(1)} %fusion.35), channel_id=1, source_target_pairs={{0,8},{2,10},{4,12},{6,14},{8,0},{10,2},{12,4},{14,6},{1,9},{3,11}... | collective-permute-start | bytes 98312 | tf_op jit(solution)/shard_map/ppermute | solution.py:18
  74.2 5.0 %collective-permute-start.34 = (bf16[16,1024]{1,0:T(8,128)(2,1)S(1)}, bf16[16,1024]{1,0:T(8,128)(2,1)S(1)}, u32[]{:S(2)}, u32[]{:S(2)}) collective-permute-start(bf16[16,1024]{1,0:T(8,128)(2,1)S(1)} %fusion.36), channel_id=1, source_target_pairs={{0,8},{2,10},{4,12},{6,14},{8,0},{10,2},{12,4},{14,6},{1,9},{3,11}... | collective-permute-start | bytes 98312 | tf_op jit(solution)/shard_map/ppermute | solution.py:18
  76.1 4.9 %collective-permute-start.37 = (bf16[16,1024]{1,0:T(8,128)(2,1)S(1)}, bf16[16,1024]{1,0:T(8,128)(2,1)S(1)}, u32[]{:S(2)}, u32[]{:S(2)}) collective-permute-start(bf16[16,1024]{1,0:T(8,128)(2,1)S(1)} %fusion.37), channel_id=1, source_target_pairs={{0,8},{2,10},{4,12},{6,14},{8,0},{10,2},{12,4},{14,6},{1,9},{3,11}... | collective-permute-start | bytes 98312 | tf_op jit(solution)/shard_map/ppermute | solution.py:18

commit v24 on v23

--- a/solution.py
+++ b/solution.py
@@ -158,9 +158,10 @@
     )
 
 
-def gram_kernel(total_cols, mine_ref, other_ref, packed_ref):
+def gram_kernel(total_cols, mine_ref, other_ref, packed_ref, sketch_ref):
     sketch = (mine_ref[...] + other_ref[...]) / total_cols
-    gram = matmul(sketch.T, sketch)
+    sketch_ref[...] = sketch.T
+    gram = matmul(sketch_ref[...], sketch)
     half = gram.shape[0] // 2
     row = lax.broadcasted_iota(jnp.int32, (half, 2 * half), 0)
     col = lax.broadcasted_iota(jnp.int32, (half, 2 * half), 1)
@@ -188,9 +189,12 @@
     rows, width = mine.shape
     return pl.pallas_call(
         functools.partial(gram_kernel, total_cols),
-        out_shape=jax.ShapeDtypeStruct((width // 2 + 8, width), jnp.float32),
+        out_shape=[
+            jax.ShapeDtypeStruct((width // 2 + 8, width), jnp.float32),
+            jax.ShapeDtypeStruct((width, rows), jnp.float32),
+        ],
         in_specs=[pl.BlockSpec(memory_space=pltpu.VMEM)] * 2,
-        out_specs=pl.BlockSpec(memory_space=pltpu.VMEM),
+        out_specs=[pl.BlockSpec(memory_space=pltpu.VMEM)] * 2,
         compiler_params=pltpu.CompilerParams(vmem_limit_bytes=16 * 2**20),
         name="make_gram",
     )(mine, other)
@@ -201,12 +205,27 @@
 CLOSE = 1e-5
 
 
-def basis_kernel(
-    total_cols, root_rows, gram_ref, mine_ref, other_ref, slab_ref,
-    basis_ref, *refs,
-):
+def pair_product(pair, slab, tile, products):
+    width = pair.shape[0] // 2
+    both = jnp.dot(pair, slab, preferred_element_type=jnp.float32)
+    out, inner = divmod(tile * TILE, products[0].shape[1])
+    products[out][:, inner : inner + TILE] = both[:width] + both[width:]
+
+
+def last_kernel(begin, pair_ref, slab_ref, *refs):
+    products, (buffer, arrived) = refs[:-2], refs[-2:]
+    copies = fetch_tiles(slab_ref, begin, buffer, arrived)
+    pair = pair_ref[...]
+    for tile, copy in enumerate(copies):
+        copy.wait()
+        pair_product(pair, buffer[tile], tile, products)
+
+
+def basis_kernel(root_rows, gram_ref, sketch_ref, slab_ref, basis_ref, pair_ref, *refs):
     products, (work_ref, inverse_ref, buffer, arrived) = refs[:-4], refs[-4:]
-    fetch = pltpu.make_async_copy(slab_ref, buffer, arrived)
+    fetch = pltpu.make_async_copy(
+        slab_ref.at[:, pl.ds(0, buffer.shape[1])], buffer, arrived
+    )
     fetch.start()
     width = gram_ref.shape[1]
     row = lax.broadcasted_iota(jnp.int32, (width, width), 0)
@@ -253,43 +272,67 @@
         pivots = jnp.sum(jnp.where(on_diag, work_ref[...], 0.0), axis=1, keepdims=True)
         inverse_ref[...] = inverse_ref[...] * lax.rsqrt(pivots)
 
-    sketch = (mine_ref[...] + other_ref[...]) / total_cols
-    basis = matmul_t(sketch, inverse_ref[...]) * root_rows
-    basis_ref[...] = basis
+    basis = matmul(inverse_ref[...], sketch_ref[...]) * root_rows
     high = basis.astype(jnp.bfloat16)
-    low = (basis - high.astype(jnp.float32)).astype(jnp.bfloat16)
-    pair = jnp.concatenate([high, low], axis=1).T
+    pair_ref[:width] = high
+    pair_ref[width:] = (basis - high.astype(jnp.float32)).astype(jnp.bfloat16)
+    pair = pair_ref[...]
     fetch.wait()
-    for start in range(0, buffer.shape[1], TILE):
-        both = lax.dot_general(
-            pair,
-            buffer[:, start : start + TILE],
-            (((1,), (0,)), ((), ())),
-            preferred_element_type=jnp.float32,
-        )
-        out, inner = divmod(start, products[0].shape[1])
-        products[out][:, inner : inner + TILE] = both[:width] + both[width:]
-
-
-def make_basis(gram, mine, other, slab, total_cols, root_rows, chunks):
-    rows, width = mine.shape
-    cols = slab.shape[1]
+    for tile in range(buffer.shape[1] // TILE):
+        slab = buffer[:, tile * TILE : (tile + 1) * TILE]
+        pair_product(pair, slab, tile, products)
+    basis_ref[...] = basis.T
+
+
+def product_shapes(width, cols, chunks):
+    return [jax.ShapeDtypeStruct((width, cols // chunks), jnp.float32)] * chunks
+
+
+def tile_scratch(rows, cols):
+    tiles = cols // TILE
+    return [pltpu.VMEM((tiles, rows, TILE), jnp.bfloat16), pltpu.SemaphoreType.DMA((tiles,))]
+
+
+def make_basis(gram, sketch, slab, cols, chunks, root_rows):
+    width, rows = sketch.shape
     return pl.pallas_call(
-        functools.partial(basis_kernel, total_cols, root_rows),
-        out_shape=[jax.ShapeDtypeStruct((rows, width), jnp.float32)]
-        + [jax.ShapeDtypeStruct((width, cols // chunks), jnp.float32)] * chunks,
-        in_specs=[pl.BlockSpec(memory_space=pltpu.VMEM)] * 3
+        functools.partial(basis_kernel, root_rows),
+        out_shape=[
+            jax.ShapeDtypeStruct((rows, width), jnp.float32),
+            jax.ShapeDtypeStruct((2 * width, rows), jnp.bfloat16),
+        ]
+        + product_shapes(width, cols, chunks),
+        in_specs=[pl.BlockSpec(memory_space=pltpu.VMEM)] * 2
         + [pl.BlockSpec(memory_space=pl.ANY)],
-        out_specs=[pl.BlockSpec(memory_space=pltpu.VMEM)] * (1 + chunks),
+        out_specs=[pl.BlockSpec(memory_space=pltpu.VMEM)] * (2 + chunks),
         scratch_shapes=[
             pltpu.VMEM((width, width), jnp.float32),
             pltpu.VMEM((width, width), jnp.float32),
-            pltpu.VMEM(slab.shape, jnp.bfloat16),
+            pltpu.VMEM((rows, cols), jnp.bfloat16),
             pltpu.SemaphoreType.DMA,
         ],
         compiler_params=pltpu.CompilerParams(vmem_limit_bytes=KERNEL_VMEM),
         name="make_basis",
-    )(gram, mine, other, slab)
+    )(gram, sketch, slab)
+
+
+def last_product(pair, slab, begin, cols, chunks):
+    twice, rows = pair.shape
+    return pl.pallas_call(
+        functools.partial(last_kernel, begin),
+        out_shape=product_shapes(twice // 2, cols, chunks),
+        in_specs=[
+            pl.BlockSpec(memory_space=pltpu.VMEM),
+            pl.BlockSpec(memory_space=pl.ANY),
+        ],
+        out_specs=[pl.BlockSpec(memory_space=pltpu.VMEM)] * chunks,
+        scratch_shapes=tile_scratch(rows, cols),
+        compiler_params=pltpu.CompilerParams(vmem_limit_bytes=KERNEL_VMEM),
+        cost_estimate=pl.CostEstimate(
+            flops=2 * rows * twice * cols, bytes_accessed=2 * rows * cols, transcendentals=0
+        ),
+        name="last_product",
+    )(pair, slab)
 
 
 def per_device(activations, start_sketch):
@@ -318,11 +361,12 @@
             preferred_element_type=jnp.float32,
         )
     other_sketch = swap(partial_sketch, "col", 1)
-    gram = row_sum(make_gram(partial_sketch, other_sketch, total_cols))
-    basis, *products = make_basis(
-        gram, partial_sketch, other_sketch, activations, total_cols, root_rows, CHUNKS
-    )
-
+    packed, sketch = make_gram(partial_sketch, other_sketch, total_cols)
+    half, chunks = cols_here // 2, CHUNKS // 2
+    basis, pair, *products = make_basis(
+        row_sum(packed), sketch, activations, half, chunks, root_rows
+    )
+    products += last_product(pair, activations, half, half, chunks)
     pieces = [
         scatter_sum(product, "row", orders[c % 2]) / total_rows
         for c, product in enumerate(products)

time: 81.9 us -> 83.6 us (1.021)
  Pallas kernels: 9.19 us -> 11.2 us
    pallas_call x2 -> x3, Pallas kernels: 5.12 us -> 7.17 us  [the longest x1 4.38 us: make_basis(): pl.pallas_call(functools.partial(basis_kernel, root_rows), out_shape=[jax...]
  transfers between devices with their start and end apart: 38 -> 38, of which waited for: 19 -> 19; matrix products, arithmetic and copies ran while one was open for 3% -> 3% of each run, Pallas kernels for 2% -> 5%
where the time goes in v24:
time: 83.6 us; the launch traced here: 83.4 us
  starting transfers between devices  44.2 us (53%)
  waiting for transfers between devices  21.9 us (26%)
  Pallas kernels  11.2 us (13%)
  other arithmetic  2.15 us (3%)
  matrix products  1.77 us (2%)
  between operations  1.12 us (1%)
  local copies, waits for them, and re-layouts  1.06 us (1%)
    ppermute x34, starting transfers between devices, swap(): return lax.ppermute(value, axis, [(i, i ^ distance) for i in range(size)])  39 us
    ppermute x34, waiting for transfers between devices, swap(): return lax.ppermute(value, axis, [(i, i ^ distance) for i in range(size)])  19.3 us
    ppermute x4, starting transfers between devices, row_sum(): terms.append(lax.ppermute(value, ('row', 'col'), pairs))  5.1 us
    pallas_call x1, Pallas kernels, make_basis(): pl.pallas_call(functools.partial(basis_kernel, root_rows), out_shape=[jax...  4.38 us
    pallas_call x2, Pallas kernels, first_product(): pl.pallas_call(functools.partial(sketch_kernel, begin), out_shape=[jax.Sh...  4.07 us
    ppermute x4, waiting for transfers between devices, row_sum(): terms.append(lax.ppermute(value, ('row', 'col'), pairs))  2.67 us
    pallas_call x1, Pallas kernels, last_product(): pl.pallas_call(functools.partial(last_kernel, begin), out_shape=product_s...  2.29 us
    dot_general x4, matrix products, per_device(): lax.dot_general(activations[:, span], shared, (((1,), (1,)), ((), ())), p...  1.77 us
  transfers between devices with their start and end apart: 38, of which 19 were waited for; matrix products, arithmetic and copies ran while one was open for 3% of the time, Pallas kernels for 5%

profile of v24, /device:TPU:0, one launch (start us, length us, event | category | flops | bytes accessed | tf_op | source)
XLA Modules:
  0.0 83.4 jit_solution(876363901751927864)
XLA Ops:
  0.7 0.9 %copy-done = bf16[512,128]{1,0:T(8,128)(2,1)S(1)} copy-done((bf16[512,128]{1,0:T(8,128)(2,1)S(1)}, bf16[512,128]{1,0:T(8,128)(2,1)}, u32[]{:S(2)}) %copy-start) | copy-done | bytes 131096
  1.6 2.1 %first_product.3 = (f32[128,1024]{1,0:T(8,128)S(1)}, f32[128,1024]{1,0:T(8,128)S(1)}) custom-call(bf16[512,128]{1,0:T(8,128)(2,1)S(1)} %copy-done, bf16[512,4096]{1,0:T(8,128)(2,1)} %slab_ref.7), custom_call_target="tpu_custom_call" | custom-call | flops 268435456 | bytes 2097152 | tf_op jit(solution)/shard_map/first_product/pallas_call | solution.py:117
  3.6 3.1 %collective-permute-start.15 = (bf16[128,512]{1,0:T(8,128)(2,1)S(1)}, bf16[128,512]{1,0:T(8,128)(2,1)S(1)}, u32[]{:S(2)}, u32[]{:S(2)}) collective-permute-start(bf16[128,512]{1,0:T(8,128)(2,1)S(1)} %select_convert_fusion.4), channel_id=1, source_target_pairs={{0,4},{2,6},{4,0},{6,2},{8,12},{10,14},{12,8},{14,10},{1,5},{3,7},... | collective-permute-start | bytes 393224 | tf_op jit(solution)/shard_map/ppermute | solution.py:18
  6.8 1.6 %collective-permute-start.10 = (bf16[128,512]{1,0:T(8,128)(2,1)S(1)}, bf16[128,512]{1,0:T(8,128)(2,1)S(1)}, u32[]{:S(2)}, u32[]{:S(2)}) collective-permute-start(bf16[128,512]{1,0:T(8,128)(2,1)S(1)} %select_convert_fusion.5), channel_id=1, source_target_pairs={{0,2},{2,0},{4,6},{6,4},{8,10},{10,8},{12,14},{14,12},{1,3},{3,1},... | collective-permute-start | bytes 393224 | tf_op jit(solution)/shard_map/ppermute | solution.py:18
  8.3 2.0 %first_product.2 = (f32[128,1024]{1,0:T(8,128)S(1)}, f32[128,1024]{1,0:T(8,128)S(1)}) custom-call(bf16[512,128]{1,0:T(8,128)(2,1)S(1)} %copy-done.1, bf16[512,4096]{1,0:T(8,128)(2,1)} %slab_ref.7), custom_call_target="tpu_custom_call" | custom-call | flops 268435456 | bytes 2097152 | tf_op jit(solution)/shard_map/first_product/pallas_call | solution.py:117
  11.2 2.0 %collective-permute-start.16 = (bf16[128,256]{1,0:T(8,128)(2,1)S(1)}, bf16[128,256]{1,0:T(8,128)(2,1)S(1)}, u32[]{:S(2)}, u32[]{:S(2)}) collective-permute-start(bf16[128,256]{1,0:T(8,128)(2,1)S(1)} %select_convert_fusion.12), channel_id=1, source_target_pairs={{0,2},{2,0},{4,6},{6,4},{8,10},{10,8},{12,14},{14,12},{1,3},{3,1},... | collective-permute-start | bytes 196616 | tf_op jit(solution)/shard_map/ppermute | solution.py:18
  13.3 1.6 %collective-permute-start.11 = (bf16[128,256]{1,0:T(8,128)(2,1)S(1)}, bf16[128,256]{1,0:T(8,128)(2,1)S(1)}, u32[]{:S(2)}, u32[]{:S(2)}) collective-permute-start(bf16[128,256]{1,0:T(8,128)(2,1)S(1)} %select_convert_fusion.13), channel_id=1, source_target_pairs={{0,4},{2,6},{4,0},{6,2},{8,12},{10,14},{12,8},{14,10},{1,5},{3,7},... | collective-permute-start | bytes 196616 | tf_op jit(solution)/shard_map/ppermute | solution.py:18
  14.9 1.2 %collective-permute-done.5 = bf16[128,512]{1,0:T(8,128)(2,1)S(1)} collective-permute-done((bf16[128,512]{1,0:T(8,128)(2,1)S(1)}, bf16[128,512]{1,0:T(8,128)(2,1)S(1)}, u32[]{:S(2)}, u32[]{:S(2)}) %collective-permute-start.5) | collective-permute-done | bytes 131104 | tf_op jit(solution)/shard_map/ppermute | solution.py:18
  16.9 1.6 %collective-permute-start.1 = (bf16[128,256]{1,0:T(8,128)(2,1)S(1)}, bf16[128,256]{1,0:T(8,128)(2,1)S(1)}, u32[]{:S(2)}, u32[]{:S(2)}) collective-permute-start(bf16[128,256]{1,0:T(8,128)(2,1)S(1)} %select_convert_fusion.15), channel_id=1, source_target_pairs={{0,4},{2,6},{4,0},{6,2},{8,12},{10,14},{12,8},{14,10},{1,5},{3,7},... | collective-permute-start | bytes 196616 | tf_op jit(solution)/shard_map/ppermute | solution.py:18
  18.6 2.7 %collective-permute-start.17 = (bf16[128,256]{1,0:T(8,128)(2,1)S(1)}, bf16[128,256]{1,0:T(8,128)(2,1)S(1)}, u32[]{:S(2)}, u32[]{:S(2)}) collective-permute-start(bf16[128,256]{1,0:T(8,128)(2,1)S(1)} %fusion.41), channel_id=1, source_target_pairs={{0,8},{2,10},{4,12},{6,14},{8,0},{10,2},{12,4},{14,6},{1,9},{3,11}... | collective-permute-start | bytes 196616 | tf_op jit(solution)/shard_map/ppermute | solution.py:18
  21.7 2.7 %collective-permute-start.7 = (bf16[128,256]{1,0:T(8,128)(2,1)S(1)}, bf16[128,256]{1,0:T(8,128)(2,1)S(1)}, u32[]{:S(2)}, u32[]{:S(2)}) collective-permute-start(bf16[128,256]{1,0:T(8,128)(2,1)S(1)} %fusion.39), channel_id=1, source_target_pairs={{0,8},{2,10},{4,12},{6,14},{8,0},{10,2},{12,4},{14,6},{1,9},{3,11}... | collective-permute-start | bytes 196616 | tf_op jit(solution)/shard_map/ppermute | solution.py:18
  24.8 2.4 %collective-permute-done.17 = bf16[128,256]{1,0:T(8,128)(2,1)S(1)} collective-permute-done((bf16[128,256]{1,0:T(8,128)(2,1)S(1)}, bf16[128,256]{1,0:T(8,128)(2,1)S(1)}, u32[]{:S(2)}, u32[]{:S(2)}) %collective-permute-start.17) | collective-permute-done | bytes 65568 | tf_op jit(solution)/shard_map/ppermute | solution.py:18
  27.2 2.7 %collective-permute-done.12 = bf16[128,256]{1,0:T(8,128)(2,1)S(1)} collective-permute-done((bf16[128,256]{1,0:T(8,128)(2,1)S(1)}, bf16[128,256]{1,0:T(8,128)(2,1)S(1)}, u32[]{:S(2)}, u32[]{:S(2)}) %collective-permute-start.12) | collective-permute-done | bytes 65568 | tf_op jit(solution)/shard_map/ppermute | solution.py:18
  30.1 0.6 collective-permute-done.7
  31.4 0.9 %collective-permute-start.3 = (bf16[128,256]{1,0:T(8,128)(2,1)S(1)}, bf16[128,256]{1,0:T(8,128)(2,1)S(1)}, u32[]{:S(2)}, u32[]{:S(2)}) collective-permute-start(bf16[128,256]{1,0:T(8,128)(2,1)S(1)} %multiply_convert_fusion.3), channel_id=1, source_target_pairs={{0,4},{2,6},{4,0},{6,2},{8,12},{10,14},{12,8},{14,10},{1,5},{3,7},... | collective-permute-start | bytes 196616 | tf_op jit(solution)/shard_map/ppermute | solution.py:18
  32.4 1.2 %collective-permute-start.19 = (bf16[128,512]{1,0:T(8,128)(2,1)S(1)}, bf16[128,512]{1,0:T(8,128)(2,1)S(1)}, u32[]{:S(2)}, u32[]{:S(2)}) collective-permute-start(bf16[128,512]{1,0:T(8,128)(2,1)S(1)} %pad_maximum_fusion.4), channel_id=1, source_target_pairs={{0,4},{2,6},{4,0},{6,2},{8,12},{10,14},{12,8},{14,10},{1,5},{3,7},... | collective-permute-start | bytes 393224 | tf_op jit(solution)/shard_map/ppermute | solution.py:18
  33.6 1.4 %collective-permute-done.13 = bf16[128,256]{1,0:T(8,128)(2,1)S(1)} collective-permute-done((bf16[128,256]{1,0:T(8,128)(2,1)S(1)}, bf16[128,256]{1,0:T(8,128)(2,1)S(1)}, u32[]{:S(2)}, u32[]{:S(2)}) %collective-permute-start.13) | collective-permute-done | bytes 65568 | tf_op jit(solution)/shard_map/ppermute | solution.py:18
  35.6 1.4 %collective-permute-start.9 = (bf16[128,512]{1,0:T(8,128)(2,1)S(1)}, bf16[128,512]{1,0:T(8,128)(2,1)S(1)}, u32[]{:S(2)}, u32[]{:S(2)}) collective-permute-start(bf16[128,512]{1,0:T(8,128)(2,1)S(1)} %pad_maximum_fusion.2), channel_id=1, source_target_pairs={{0,4},{2,6},{4,0},{6,2},{8,12},{10,14},{12,8},{14,10},{1,5},{3,7},... | collective-permute-start | bytes 393224 | tf_op jit(solution)/shard_map/ppermute | solution.py:18
  37.1 0.9 %collective-permute-start.4 = (bf16[128,512]{1,0:T(8,128)(2,1)S(1)}, bf16[128,512]{1,0:T(8,128)(2,1)S(1)}, u32[]{:S(2)}, u32[]{:S(2)}) collective-permute-start(bf16[128,512]{1,0:T(8,128)(2,1)S(1)} %pad_maximum_fusion.1), channel_id=1, source_target_pairs={{0,2},{2,0},{4,6},{6,4},{8,10},{10,8},{12,14},{14,12},{1,3},{3,1},... | collective-permute-start | bytes 393224 | tf_op jit(solution)/shard_map/ppermute | solution.py:18
  38.0 1.1 %collective-permute-done.19 = bf16[128,512]{1,0:T(8,128)(2,1)S(1)} collective-permute-done((bf16[128,512]{1,0:T(8,128)(2,1)S(1)}, bf16[128,512]{1,0:T(8,128)(2,1)S(1)}, u32[]{:S(2)}, u32[]{:S(2)}) %collective-permute-start.19) | collective-permute-done | bytes 131104 | tf_op jit(solution)/shard_map/ppermute | solution.py:18
  41.2 1.0 %collective-permute-done.4 = bf16[128,512]{1,0:T(8,128)(2,1)S(1)} collective-permute-done((bf16[128,512]{1,0:T(8,128)(2,1)S(1)}, bf16[128,512]{1,0:T(8,128)(2,1)S(1)}, u32[]{:S(2)}, u32[]{:S(2)}) %collective-permute-start.4) | collective-permute-done | bytes 131104 | tf_op jit(solution)/shard_map/ppermute | solution.py:18
  42.7 1.5 %collective-permute-done.20.other_ref = f32[512,128]{1,0:T(8,128)S(1)} collective-permute-done((f32[512,128]{1,0:T(8,128)S(1)}, f32[512,128]{1,0:T(8,128)S(1)}, u32[]{:S(2)}, u32[]{:S(2)}) %collective-permute-start.20) | collective-permute-done | bytes 262176 | tf_op jit(solution)/shard_map/ppermute | solution.py:18
  44.7 2.3 %collective-permute-start.24 = (f32[72,128]{1,0:T(8,128)S(1)}, f32[72,128]{1,0:T(8,128)S(1)}, u32[]{:S(2)}, u32[]{:S(2)}) collective-permute-start(f32[72,128]{1,0:T(8,128)S(1)} %get-tuple-element.18), channel_id=1, source_target_pairs={{0,10},{1,15},{2,8},{3,13},{4,14},{5,11},{6,12},{7,9},{8,2},{9,7},... | collective-permute-start | bytes 110600 | tf_op jit(solution)/shard_map/ppermute | solution.py:36
  47.0 0.9 %collective-permute-start.23 = (f32[72,128]{1,0:T(8,128)S(1)}, f32[72,128]{1,0:T(8,128)S(1)}, u32[]{:S(2)}, u32[]{:S(2)}) collective-permute-start(f32[72,128]{1,0:T(8,128)S(1)} %get-tuple-element.18), channel_id=1, source_target_pairs={{0,8},{1,13},{2,10},{3,15},{4,12},{5,9},{6,14},{7,11},{8,0},{9,5},... | collective-permute-start | bytes 110600 | tf_op jit(solution)/shard_map/ppermute | solution.py:36
  48.0 1.2 %collective-permute-start.22 = (f32[72,128]{1,0:T(8,128)S(1)}, f32[72,128]{1,0:T(8,128)S(1)}, u32[]{:S(2)}, u32[]{:S(2)}) collective-permute-start(f32[72,128]{1,0:T(8,128)S(1)} %get-tuple-element.18), channel_id=1, source_target_pairs={{0,2},{1,7},{2,0},{3,5},{4,6},{5,3},{6,4},{7,1},{8,10},{9,15},{10,... | collective-permute-start | bytes 110600 | tf_op jit(solution)/shard_map/ppermute | solution.py:36
  49.2 0.7 collective-permute-start.21
  49.9 1.5 %collective-permute-done.24 = f32[72,128]{1,0:T(8,128)S(1)} collective-permute-done((f32[72,128]{1,0:T(8,128)S(1)}, f32[72,128]{1,0:T(8,128)S(1)}, u32[]{:S(2)}, u32[]{:S(2)}) %collective-permute-start.24) | collective-permute-done | bytes 36896 | tf_op jit(solution)/shard_map/ppermute | solution.py:36
  51.4 1.2 %collective-permute-done.23 = f32[72,128]{1,0:T(8,128)S(1)} collective-permute-done((f32[72,128]{1,0:T(8,128)S(1)}, f32[72,128]{1,0:T(8,128)S(1)}, u32[]{:S(2)}, u32[]{:S(2)}) %collective-permute-start.23) | collective-permute-done | bytes 36896 | tf_op jit(solution)/shard_map/ppermute | solution.py:36
  52.5 1.3 %collective-permute-start.25 = (f32[72,128]{1,0:T(8,128)S(1)}, f32[72,128]{1,0:T(8,128)S(1)}, u32[]{:S(2)}, u32[]{:S(2)}) collective-permute-start(f32[72,128]{1,0:T(8,128)S(1)} %add_add_fusion), channel_id=1, source_target_pairs={{0,1},{1,0},{2,3},{3,2},{4,5},{5,4},{6,7},{7,6},{8,9},{9,8},{10,11... | collective-permute-start | bytes 110600 | tf_op jit(solution)/shard_map/ppermute | solution.py:18
  53.9 0.9 %collective-permute-done.25 = f32[72,128]{1,0:T(8,128)S(1)} collective-permute-done((f32[72,128]{1,0:T(8,128)S(1)}, f32[72,128]{1,0:T(8,128)S(1)}, u32[]{:S(2)}, u32[]{:S(2)}) %collective-permute-start.25) | collective-permute-done | bytes 36896 | tf_op jit(solution)/shard_map/ppermute | solution.py:18
  54.8 4.4 %make_basis.1 = (f32[512,128]{1,0:T(8,128)}, bf16[256,512]{1,0:T(8,128)(2,1)S(1)}, f32[128,1024]{1,0:T(8,128)S(1)}, f32[128,1024]{1,0:T(8,128)S(1)}) custom-call(f32[72,128]{1,0:T(8,128)S(1)} %add.116.gram_ref, f32[128,512]{1,0:T(8,128)S(1)} %get-tuple-element.19.sketch_ref, bf16[512,4096]{1,0:T(8,128)(2,1)} %slab_ref.7), custom_call_target="tpu_custom_call" | custom-call | tf_op jit(solution)/shard_map/make_basis/pallas_call | solution.py:298
  59.2 0.9 %collective-permute-start.26 = (bf16[2,2,16,1024]{3,2,0,1:T(8,128)(2,1)S(1)}, bf16[2,2,16,1024]{3,2,0,1:T(8,128)(2,1)S(1)}, u32[]{:S(2)}, u32[]{:S(2)}) collective-permute-start(bf16[2,2,16,1024]{3,2,0,1:T(8,128)(2,1)S(1)} %fusion.22), channel_id=1, source_target_pairs={{0,2},{2,0},{4,6},{6,4},{8,10},{10,8},{12,14},{14,12},{1,3},{3,1},... | collective-permute-start | bytes 393224 | tf_op jit(solution)/shard_map/ppermute | solution.py:18
  60.2 1.8 %collective-permute-start.29 = (bf16[2,2,16,1024]{3,2,0,1:T(8,128)(2,1)S(1)}, bf16[2,2,16,1024]{3,2,0,1:T(8,128)(2,1)S(1)}, u32[]{:S(2)}, u32[]{:S(2)}) collective-permute-start(bf16[2,2,16,1024]{3,2,0,1:T(8,128)(2,1)S(1)} %fusion.23), channel_id=1, source_target_pairs={{0,4},{2,6},{4,0},{6,2},{8,12},{10,14},{12,8},{14,10},{1,5},{3,7},... | collective-permute-start | bytes 393224 | tf_op jit(solution)/shard_map/ppermute | solution.py:18
  62.0 2.3 %last_product.1 = (f32[128,1024]{1,0:T(8,128)S(1)}, f32[128,1024]{1,0:T(8,128)S(1)}) custom-call(bf16[256,512]{1,0:T(8,128)(2,1)S(1)} %get-tuple-element.23.pair_ref, bf16[512,4096]{1,0:T(8,128)(2,1)} %slab_ref.7), custom_call_target="tpu_custom_call" | custom-call | flops 536870912 | bytes 2097152 | tf_op jit(solution)/shard_map/last_product/pallas_call | solution.py:321
  64.8 1.3 %collective-permute-start.32 = (bf16[2,2,16,1024]{3,2,0,1:T(8,128)(2,1)S(1)}, bf16[2,2,16,1024]{3,2,0,1:T(8,128)(2,1)S(1)}, u32[]{:S(2)}, u32[]{:S(2)}) collective-permute-start(bf16[2,2,16,1024]{3,2,0,1:T(8,128)(2,1)S(1)} %fusion.24), channel_id=1, source_target_pairs={{0,2},{2,0},{4,6},{6,4},{8,10},{10,8},{12,14},{14,12},{1,3},{3,1},... | collective-permute-start | bytes 393224 | tf_op jit(solution)/shard_map/ppermute | solution.py:18
  66.2 1.8 %collective-permute-start.27 = (bf16[2,16,1024]{2,1,0:T(8,128)(2,1)S(1)}, bf16[2,16,1024]{2,1,0:T(8,128)(2,1)S(1)}, u32[]{:S(2)}, u32[]{:S(2)}) collective-permute-start(bf16[2,16,1024]{2,1,0:T(8,128)(2,1)S(1)} %fusion.26), channel_id=1, source_target_pairs={{0,4},{2,6},{4,0},{6,2},{8,12},{10,14},{12,8},{14,10},{1,5},{3,7},... | collective-permute-start | bytes 196616 | tf_op jit(solution)/shard_map/ppermute | solution.py:18
  68.0 0.9 %collective-permute-start.30 = (bf16[2,16,1024]{2,1,0:T(8,128)(2,1)S(1)}, bf16[2,16,1024]{2,1,0:T(8,128)(2,1)S(1)}, u32[]{:S(2)}, u32[]{:S(2)}) collective-permute-start(bf16[2,16,1024]{2,1,0:T(8,128)(2,1)S(1)} %fusion.27), channel_id=1, source_target_pairs={{0,2},{2,0},{4,6},{6,4},{8,10},{10,8},{12,14},{14,12},{1,3},{3,1},... | collective-permute-start | bytes 196616 | tf_op jit(solution)/shard_map/ppermute | solution.py:18
  68.9 1.5 %collective-permute-done.35 = bf16[2,2,16,1024]{3,2,0,1:T(8,128)(2,1)S(1)} collective-permute-done((bf16[2,2,16,1024]{3,2,0,1:T(8,128)(2,1)S(1)}, bf16[2,2,16,1024]{3,2,0,1:T(8,128)(2,1)S(1)}, u32[]{:S(2)}, u32[]{:S(2)}) %collective-permute-start.35) | collective-permute-done | bytes 131104 | tf_op jit(solution)/shard_map/ppermute | solution.py:18
  70.5 1.3 %collective-permute-start.36 = (bf16[2,16,1024]{2,1,0:T(8,128)(2,1)S(1)}, bf16[2,16,1024]{2,1,0:T(8,128)(2,1)S(1)}, u32[]{:S(2)}, u32[]{:S(2)}) collective-permute-start(bf16[2,16,1024]{2,1,0:T(8,128)(2,1)S(1)} %fusion.29), channel_id=1, source_target_pairs={{0,2},{2,0},{4,6},{6,4},{8,10},{10,8},{12,14},{14,12},{1,3},{3,1},... | collective-permute-start | bytes 196616 | tf_op jit(solution)/shard_map/ppermute | solution.py:18
  71.8 0.7 collective-permute-start.33
  72.5 1.7 %collective-permute-start.28 = (bf16[16,1024]{1,0:T(8,128)(2,1)S(1)}, bf16[16,1024]{1,0:T(8,128)(2,1)S(1)}, u32[]{:S(2)}, u32[]{:S(2)}) collective-permute-start(bf16[16,1024]{1,0:T(8,128)(2,1)S(1)} %fusion.34), channel_id=1, source_target_pairs={{0,8},{2,10},{4,12},{6,14},{8,0},{10,2},{12,4},{14,6},{1,9},{3,11}... | collective-permute-start | bytes 98312 | tf_op jit(solution)/shard_map/ppermute | solution.py:18
  74.3 1.3 %collective-permute-start.31 = (bf16[16,1024]{1,0:T(8,128)(2,1)S(1)}, bf16[16,1024]{1,0:T(8,128)(2,1)S(1)}, u32[]{:S(2)}, u32[]{:S(2)}) collective-permute-start(bf16[16,1024]{1,0:T(8,128)(2,1)S(1)} %fusion.35), channel_id=1, source_target_pairs={{0,8},{2,10},{4,12},{6,14},{8,0},{10,2},{12,4},{14,6},{1,9},{3,11}... | collective-permute-start | bytes 98312 | tf_op jit(solution)/shard_map/ppermute | solution.py:18
  75.7 1.7 %collective-permute-start.37 = (bf16[16,1024]{1,0:T(8,128)(2,1)S(1)}, bf16[16,1024]{1,0:T(8,128)(2,1)S(1)}, u32[]{:S(2)}, u32[]{:S(2)}) collective-permute-start(bf16[16,1024]{1,0:T(8,128)(2,1)S(1)} %fusion.37), channel_id=1, source_target_pairs={{0,8},{2,10},{4,12},{6,14},{8,0},{10,2},{12,4},{14,6},{1,9},{3,11}... | collective-permute-start | bytes 98312 | tf_op jit(solution)/shard_map/ppermute | solution.py:18
  77.5 1.3 %collective-permute-start.34 = (bf16[16,1024]{1,0:T(8,128)(2,1)S(1)}, bf16[16,1024]{1,0:T(8,128)(2,1)S(1)}, u32[]{:S(2)}, u32[]{:S(2)}) collective-permute-start(bf16[16,1024]{1,0:T(8,128)(2,1)S(1)} %fusion.36), channel_id=1, source_target_pairs={{0,8},{2,10},{4,12},{6,14},{8,0},{10,2},{12,4},{14,6},{1,9},{3,11}... | collective-permute-start | bytes 98312 | tf_op jit(solution)/shard_map/ppermute | solution.py:18
  78.8 0.8 collective-permute-done.31
  79.6 0.9 %collective-permute-done.37 = bf16[16,1024]{1,0:T(8,128)(2,1)S(1)} collective-permute-done((bf16[16,1024]{1,0:T(8,128)(2,1)S(1)}, bf16[16,1024]{1,0:T(8,128)(2,1)S(1)}, u32[]{:S(2)}, u32[]{:S(2)}) %collective-permute-start.37) | collective-permute-done | bytes 32800 | tf_op jit(solution)/shard_map/ppermute | solution.py:18
  80.6 2.1 %collective-permute-done.34 = bf16[16,1024]{1,0:T(8,128)(2,1)S(1)} collective-permute-done((bf16[16,1024]{1,0:T(8,128)(2,1)S(1)}, bf16[16,1024]{1,0:T(8,128)(2,1)S(1)}, u32[]{:S(2)}, u32[]{:S(2)}) %collective-permute-start.34) | collective-permute-done | bytes 32800 | tf_op jit(solution)/shard_map/ppermute | solution.py:18
  82.7 0.7 pad_maximum_fusion
  (106 shorter events, 8.4 us)
Async XLA Ops:
  0.6 0.9 %copy-start = (bf16[512,128]{1,0:T(8,128)(2,1)S(1)}, bf16[512,128]{1,0:T(8,128)(2,1)}, u32[]{:S(2)}) copy-start(bf16[512,128]{1,0:T(8,128)(2,1)} %start_ref.3) | copy-start | bytes 393220
  1.6 6.8 %copy-start.1 = (bf16[512,128]{1,0:T(8,128)(2,1)S(1)}, bf16[512,128]{1,0:T(8,128)(2,1)}, u32[]{:S(2)}) copy-start(bf16[512,128]{1,0:T(8,128)(2,1)} %start_ref.3) | copy-start | bytes 393220
  3.6 7.5 %collective-permute-start.15 = (bf16[128,512]{1,0:T(8,128)(2,1)S(1)}, bf16[128,512]{1,0:T(8,128)(2,1)S(1)}, u32[]{:S(2)}, u32[]{:S(2)}) collective-permute-start(bf16[128,512]{1,0:T(8,128)(2,1)S(1)} %select_convert_fusion.4), channel_id=1, source_target_pairs={{0,4},{2,6},{4,0},{6,2},{8,12},{10,14},{12,8},{14,10},{1,5},{3,7},... | collective-permute-start | bytes 393224 | tf_op jit(solution)/shard_map/ppermute | solution.py:18
  6.8 6.4 %collective-permute-start.10 = (bf16[128,512]{1,0:T(8,128)(2,1)S(1)}, bf16[128,512]{1,0:T(8,128)(2,1)S(1)}, u32[]{:S(2)}, u32[]{:S(2)}) collective-permute-start(bf16[128,512]{1,0:T(8,128)(2,1)S(1)} %select_convert_fusion.5), channel_id=1, source_target_pairs={{0,2},{2,0},{4,6},{6,4},{8,10},{10,8},{12,14},{14,12},{1,3},{3,1},... | collective-permute-start | bytes 393224 | tf_op jit(solution)/shard_map/ppermute | solution.py:18
  10.4 5.7 %collective-permute-start.5 = (bf16[128,512]{1,0:T(8,128)(2,1)S(1)}, bf16[128,512]{1,0:T(8,128)(2,1)S(1)}, u32[]{:S(2)}, u32[]{:S(2)}) collective-permute-start(bf16[128,512]{1,0:T(8,128)(2,1)S(1)} %select_convert_fusion.6), channel_id=1, source_target_pairs={{0,4},{2,6},{4,0},{6,2},{8,12},{10,14},{12,8},{14,10},{1,5},{3,7},... | collective-permute-start | bytes 393224 | tf_op jit(solution)/shard_map/ppermute | solution.py:18
  10.9 5.9 %collective-permute-start = (bf16[128,512]{1,0:T(8,128)(2,1)S(1)}, bf16[128,512]{1,0:T(8,128)(2,1)S(1)}, u32[]{:S(2)}, u32[]{:S(2)}) collective-permute-start(bf16[128,512]{1,0:T(8,128)(2,1)S(1)} %select_convert_fusion.7), channel_id=1, source_target_pairs={{0,2},{2,0},{4,6},{6,4},{8,10},{10,8},{12,14},{14,12},{1,3},{3,1},... | collective-permute-start | bytes 393224 | tf_op jit(solution)/shard_map/ppermute | solution.py:18
  11.2 7.3 %collective-permute-start.16 = (bf16[128,256]{1,0:T(8,128)(2,1)S(1)}, bf16[128,256]{1,0:T(8,128)(2,1)S(1)}, u32[]{:S(2)}, u32[]{:S(2)}) collective-permute-start(bf16[128,256]{1,0:T(8,128)(2,1)S(1)} %select_convert_fusion.12), channel_id=1, source_target_pairs={{0,2},{2,0},{4,6},{6,4},{8,10},{10,8},{12,14},{14,12},{1,3},{3,1},... | collective-permute-start | bytes 196616 | tf_op jit(solution)/shard_map/ppermute | solution.py:18
  13.2 25.9 %copy-start.2 = (bf16[512,4096]{1,0:T(8,128)(2,1)S(1)}, bf16[512,4096]{1,0:T(8,128)(2,1)}, u32[]{:S(2)}) copy-start(bf16[512,4096]{1,0:T(8,128)(2,1)} %slab_ref.7) | copy-start | bytes 12582916
  13.3 8.0 %collective-permute-start.11 = (bf16[128,256]{1,0:T(8,128)(2,1)S(1)}, bf16[128,256]{1,0:T(8,128)(2,1)S(1)}, u32[]{:S(2)}, u32[]{:S(2)}) collective-permute-start(bf16[128,256]{1,0:T(8,128)(2,1)S(1)} %select_convert_fusion.13), channel_id=1, source_target_pairs={{0,4},{2,6},{4,0},{6,2},{8,12},{10,14},{12,8},{14,10},{1,5},{3,7},... | collective-permute-start | bytes 196616 | tf_op jit(solution)/shard_map/ppermute | solution.py:18
  16.2 5.4 %collective-permute-start.6 = (bf16[128,256]{1,0:T(8,128)(2,1)S(1)}, bf16[128,256]{1,0:T(8,128)(2,1)S(1)}, u32[]{:S(2)}, u32[]{:S(2)}) collective-permute-start(bf16[128,256]{1,0:T(8,128)(2,1)S(1)} %select_convert_fusion.14), channel_id=1, source_target_pairs={{0,2},{2,0},{4,6},{6,4},{8,10},{10,8},{12,14},{14,12},{1,3},{3,1},... | collective-permute-start | bytes 196616 | tf_op jit(solution)/shard_map/ppermute | solution.py:18
  16.9 7.4 %collective-permute-start.1 = (bf16[128,256]{1,0:T(8,128)(2,1)S(1)}, bf16[128,256]{1,0:T(8,128)(2,1)S(1)}, u32[]{:S(2)}, u32[]{:S(2)}) collective-permute-start(bf16[128,256]{1,0:T(8,128)(2,1)S(1)} %select_convert_fusion.15), channel_id=1, source_target_pairs={{0,4},{2,6},{4,0},{6,2},{8,12},{10,14},{12,8},{14,10},{1,5},{3,7},... | collective-permute-start | bytes 196616 | tf_op jit(solution)/shard_map/ppermute | solution.py:18
  18.6 8.6 %collective-permute-start.17 = (bf16[128,256]{1,0:T(8,128)(2,1)S(1)}, bf16[128,256]{1,0:T(8,128)(2,1)S(1)}, u32[]{:S(2)}, u32[]{:S(2)}) collective-permute-start(bf16[128,256]{1,0:T(8,128)(2,1)S(1)} %fusion.41), channel_id=1, source_target_pairs={{0,8},{2,10},{4,12},{6,14},{8,0},{10,2},{12,4},{14,6},{1,9},{3,11}... | collective-permute-start | bytes 196616 | tf_op jit(solution)/shard_map/ppermute | solution.py:18
  21.2 8.7 %collective-permute-start.12 = (bf16[128,256]{1,0:T(8,128)(2,1)S(1)}, bf16[128,256]{1,0:T(8,128)(2,1)S(1)}, u32[]{:S(2)}, u32[]{:S(2)}) collective-permute-start(bf16[128,256]{1,0:T(8,128)(2,1)S(1)} %fusion.40), channel_id=1, source_target_pairs={{0,8},{2,10},{4,12},{6,14},{8,0},{10,2},{12,4},{14,6},{1,9},{3,11}... | collective-permute-start | bytes 196616 | tf_op jit(solution)/shard_map/ppermute | solution.py:18
  21.7 9.0 %collective-permute-start.7 = (bf16[128,256]{1,0:T(8,128)(2,1)S(1)}, bf16[128,256]{1,0:T(8,128)(2,1)S(1)}, u32[]{:S(2)}, u32[]{:S(2)}) collective-permute-start(bf16[128,256]{1,0:T(8,128)(2,1)S(1)} %fusion.39), channel_id=1, source_target_pairs={{0,8},{2,10},{4,12},{6,14},{8,0},{10,2},{12,4},{14,6},{1,9},{3,11}... | collective-permute-start | bytes 196616 | tf_op jit(solution)/shard_map/ppermute | solution.py:18
  24.4 7.0 %collective-permute-start.2 = (bf16[128,256]{1,0:T(8,128)(2,1)S(1)}, bf16[128,256]{1,0:T(8,128)(2,1)S(1)}, u32[]{:S(2)}, u32[]{:S(2)}) collective-permute-start(bf16[128,256]{1,0:T(8,128)(2,1)S(1)} %fusion.38), channel_id=1, source_target_pairs={{0,8},{2,10},{4,12},{6,14},{8,0},{10,2},{12,4},{14,6},{1,9},{3,11}... | collective-permute-start | bytes 196616 | tf_op jit(solution)/shard_map/ppermute | solution.py:18
  27.2 5.2 %collective-permute-start.18 = (bf16[128,256]{1,0:T(8,128)(2,1)S(1)}, bf16[128,256]{1,0:T(8,128)(2,1)S(1)}, u32[]{:S(2)}, u32[]{:S(2)}) collective-permute-start(bf16[128,256]{1,0:T(8,128)(2,1)S(1)} %multiply_convert_fusion), channel_id=1, source_target_pairs={{0,2},{2,0},{4,6},{6,4},{8,10},{10,8},{12,14},{14,12},{1,3},{3,1},... | collective-permute-start | bytes 196616 | tf_op jit(solution)/shard_map/ppermute | solution.py:18
  30.0 5.0 %collective-permute-start.13 = (bf16[128,256]{1,0:T(8,128)(2,1)S(1)}, bf16[128,256]{1,0:T(8,128)(2,1)S(1)}, u32[]{:S(2)}, u32[]{:S(2)}) collective-permute-start(bf16[128,256]{1,0:T(8,128)(2,1)S(1)} %multiply_convert_fusion.1), channel_id=1, source_target_pairs={{0,4},{2,6},{4,0},{6,2},{8,12},{10,14},{12,8},{14,10},{1,5},{3,7},... | collective-permute-start | bytes 196616 | tf_op jit(solution)/shard_map/ppermute | solution.py:18
  30.7 4.9 %collective-permute-start.8 = (bf16[128,256]{1,0:T(8,128)(2,1)S(1)}, bf16[128,256]{1,0:T(8,128)(2,1)S(1)}, u32[]{:S(2)}, u32[]{:S(2)}) collective-permute-start(bf16[128,256]{1,0:T(8,128)(2,1)S(1)} %multiply_convert_fusion.2), channel_id=1, source_target_pairs={{0,2},{2,0},{4,6},{6,4},{8,10},{10,8},{12,14},{14,12},{1,3},{3,1},... | collective-permute-start | bytes 196616 | tf_op jit(solution)/shard_map/ppermute | solution.py:18
  31.4 5.6 %collective-permute-start.3 = (bf16[128,256]{1,0:T(8,128)(2,1)S(1)}, bf16[128,256]{1,0:T(8,128)(2,1)S(1)}, u32[]{:S(2)}, u32[]{:S(2)}) collective-permute-start(bf16[128,256]{1,0:T(8,128)(2,1)S(1)} %multiply_convert_fusion.3), channel_id=1, source_target_pairs={{0,4},{2,6},{4,0},{6,2},{8,12},{10,14},{12,8},{14,10},{1,5},{3,7},... | collective-permute-start | bytes 196616 | tf_op jit(solution)/shard_map/ppermute | solution.py:18
  32.4 6.8 %collective-permute-start.19 = (bf16[128,512]{1,0:T(8,128)(2,1)S(1)}, bf16[128,512]{1,0:T(8,128)(2,1)S(1)}, u32[]{:S(2)}, u32[]{:S(2)}) collective-permute-start(bf16[128,512]{1,0:T(8,128)(2,1)S(1)} %pad_maximum_fusion.4), channel_id=1, source_target_pairs={{0,4},{2,6},{4,0},{6,2},{8,12},{10,14},{12,8},{14,10},{1,5},{3,7},... | collective-permute-start | bytes 393224 | tf_op jit(solution)/shard_map/ppermute | solution.py:18
  35.0 5.0 %collective-permute-start.14 = (bf16[128,512]{1,0:T(8,128)(2,1)S(1)}, bf16[128,512]{1,0:T(8,128)(2,1)S(1)}, u32[]{:S(2)}, u32[]{:S(2)}) collective-permute-start(bf16[128,512]{1,0:T(8,128)(2,1)S(1)} %pad_maximum_fusion.3), channel_id=1, source_target_pairs={{0,2},{2,0},{4,6},{6,4},{8,10},{10,8},{12,14},{14,12},{1,3},{3,1},... | collective-permute-start | bytes 393224 | tf_op jit(solution)/shard_map/ppermute | solution.py:18
  35.6 5.0 %collective-permute-start.9 = (bf16[128,512]{1,0:T(8,128)(2,1)S(1)}, bf16[128,512]{1,0:T(8,128)(2,1)S(1)}, u32[]{:S(2)}, u32[]{:S(2)}) collective-permute-start(bf16[128,512]{1,0:T(8,128)(2,1)S(1)} %pad_maximum_fusion.2), channel_id=1, source_target_pairs={{0,4},{2,6},{4,0},{6,2},{8,12},{10,14},{12,8},{14,10},{1,5},{3,7},... | collective-permute-start | bytes 393224 | tf_op jit(solution)/shard_map/ppermute | solution.py:18
  37.1 5.0 %collective-permute-start.4 = (bf16[128,512]{1,0:T(8,128)(2,1)S(1)}, bf16[128,512]{1,0:T(8,128)(2,1)S(1)}, u32[]{:S(2)}, u32[]{:S(2)}) collective-permute-start(bf16[128,512]{1,0:T(8,128)(2,1)S(1)} %pad_maximum_fusion.1), channel_id=1, source_target_pairs={{0,2},{2,0},{4,6},{6,4},{8,10},{10,8},{12,14},{14,12},{1,3},{3,1},... | collective-permute-start | bytes 393224 | tf_op jit(solution)/shard_map/ppermute | solution.py:18
  42.6 1.6 %collective-permute-start.20 = (f32[512,128]{1,0:T(8,128)S(1)}, f32[512,128]{1,0:T(8,128)S(1)}, u32[]{:S(2)}, u32[]{:S(2)}) collective-permute-start(f32[512,128]{1,0:T(8,128)S(1)} %fusion.2.mine_ref), channel_id=1, source_target_pairs={{0,1},{1,0},{2,3},{3,2},{4,5},{5,4},{6,7},{7,6},{8,9},{9,8},{10,11... | collective-permute-start | bytes 786440 | tf_op jit(solution)/shard_map/ppermute | solution.py:18
  44.7 6.6 %collective-permute-start.24 = (f32[72,128]{1,0:T(8,128)S(1)}, f32[72,128]{1,0:T(8,128)S(1)}, u32[]{:S(2)}, u32[]{:S(2)}) collective-permute-start(f32[72,128]{1,0:T(8,128)S(1)} %get-tuple-element.18), channel_id=1, source_target_pairs={{0,10},{1,15},{2,8},{3,13},{4,14},{5,11},{6,12},{7,9},{8,2},{9,7},... | collective-permute-start | bytes 110600 | tf_op jit(solution)/shard_map/ppermute | solution.py:36
  47.0 5.5 %collective-permute-start.23 = (f32[72,128]{1,0:T(8,128)S(1)}, f32[72,128]{1,0:T(8,128)S(1)}, u32[]{:S(2)}, u32[]{:S(2)}) collective-permute-start(f32[72,128]{1,0:T(8,128)S(1)} %get-tuple-element.18), channel_id=1, source_target_pairs={{0,8},{1,13},{2,10},{3,15},{4,12},{5,9},{6,14},{7,11},{8,0},{9,5},... | collective-permute-start | bytes 110600 | tf_op jit(solution)/shard_map/ppermute | solution.py:36
  48.0 4.5 %collective-permute-start.22 = (f32[72,128]{1,0:T(8,128)S(1)}, f32[72,128]{1,0:T(8,128)S(1)}, u32[]{:S(2)}, u32[]{:S(2)}) collective-permute-start(f32[72,128]{1,0:T(8,128)S(1)} %get-tuple-element.18), channel_id=1, source_target_pairs={{0,2},{1,7},{2,0},{3,5},{4,6},{5,3},{6,4},{7,1},{8,10},{9,15},{10,... | collective-permute-start | bytes 110600 | tf_op jit(solution)/shard_map/ppermute | solution.py:36
  49.2 3.3 %collective-permute-start.21 = (f32[72,128]{1,0:T(8,128)S(1)}, f32[72,128]{1,0:T(8,128)S(1)}, u32[]{:S(2)}, u32[]{:S(2)}) collective-permute-start(f32[72,128]{1,0:T(8,128)S(1)} %get-tuple-element.18), channel_id=1, source_target_pairs={{1,5},{3,7},{5,1},{7,3},{9,13},{11,15},{13,9},{15,11},{17,21},{19,... | collective-permute-start | bytes 110600 | tf_op jit(solution)/shard_map/ppermute | solution.py:36
  52.5 2.2 %collective-permute-start.25 = (f32[72,128]{1,0:T(8,128)S(1)}, f32[72,128]{1,0:T(8,128)S(1)}, u32[]{:S(2)}, u32[]{:S(2)}) collective-permute-start(f32[72,128]{1,0:T(8,128)S(1)} %add_add_fusion), channel_id=1, source_target_pairs={{0,1},{1,0},{2,3},{3,2},{4,5},{5,4},{6,7},{7,6},{8,9},{9,8},{10,11... | collective-permute-start | bytes 110600 | tf_op jit(solution)/shard_map/ppermute | solution.py:18
  59.2 6.9 %collective-permute-start.26 = (bf16[2,2,16,1024]{3,2,0,1:T(8,128)(2,1)S(1)}, bf16[2,2,16,1024]{3,2,0,1:T(8,128)(2,1)S(1)}, u32[]{:S(2)}, u32[]{:S(2)}) collective-permute-start(bf16[2,2,16,1024]{3,2,0,1:T(8,128)(2,1)S(1)} %fusion.22), channel_id=1, source_target_pairs={{0,2},{2,0},{4,6},{6,4},{8,10},{10,8},{12,14},{14,12},{1,3},{3,1},... | collective-permute-start | bytes 393224 | tf_op jit(solution)/shard_map/ppermute | solution.py:18
  60.2 7.8 %collective-permute-start.29 = (bf16[2,2,16,1024]{3,2,0,1:T(8,128)(2,1)S(1)}, bf16[2,2,16,1024]{3,2,0,1:T(8,128)(2,1)S(1)}, u32[]{:S(2)}, u32[]{:S(2)}) collective-permute-start(bf16[2,2,16,1024]{3,2,0,1:T(8,128)(2,1)S(1)} %fusion.23), channel_id=1, source_target_pairs={{0,4},{2,6},{4,0},{6,2},{8,12},{10,14},{12,8},{14,10},{1,5},{3,7},... | collective-permute-start | bytes 393224 | tf_op jit(solution)/shard_map/ppermute | solution.py:18
  64.4 6.0 %collective-permute-start.35 = (bf16[2,2,16,1024]{3,2,0,1:T(8,128)(2,1)S(1)}, bf16[2,2,16,1024]{3,2,0,1:T(8,128)(2,1)S(1)}, u32[]{:S(2)}, u32[]{:S(2)}) collective-permute-start(bf16[2,2,16,1024]{3,2,0,1:T(8,128)(2,1)S(1)} %fusion.25), channel_id=1, source_target_pairs={{0,4},{2,6},{4,0},{6,2},{8,12},{10,14},{12,8},{14,10},{1,5},{3,7},... | collective-permute-start | bytes 393224 | tf_op jit(solution)/shard_map/ppermute | solution.py:18
  64.8 6.9 %collective-permute-start.32 = (bf16[2,2,16,1024]{3,2,0,1:T(8,128)(2,1)S(1)}, bf16[2,2,16,1024]{3,2,0,1:T(8,128)(2,1)S(1)}, u32[]{:S(2)}, u32[]{:S(2)}) collective-permute-start(bf16[2,2,16,1024]{3,2,0,1:T(8,128)(2,1)S(1)} %fusion.24), channel_id=1, source_target_pairs={{0,2},{2,0},{4,6},{6,4},{8,10},{10,8},{12,14},{14,12},{1,3},{3,1},... | collective-permute-start | bytes 393224 | tf_op jit(solution)/shard_map/ppermute | solution.py:18
  66.2 6.3 %collective-permute-start.27 = (bf16[2,16,1024]{2,1,0:T(8,128)(2,1)S(1)}, bf16[2,16,1024]{2,1,0:T(8,128)(2,1)S(1)}, u32[]{:S(2)}, u32[]{:S(2)}) collective-permute-start(bf16[2,16,1024]{2,1,0:T(8,128)(2,1)S(1)} %fusion.26), channel_id=1, source_target_pairs={{0,4},{2,6},{4,0},{6,2},{8,12},{10,14},{12,8},{14,10},{1,5},{3,7},... | collective-permute-start | bytes 196616 | tf_op jit(solution)/shard_map/ppermute | solution.py:18
  68.0 6.2 %collective-permute-start.30 = (bf16[2,16,1024]{2,1,0:T(8,128)(2,1)S(1)}, bf16[2,16,1024]{2,1,0:T(8,128)(2,1)S(1)}, u32[]{:S(2)}, u32[]{:S(2)}) collective-permute-start(bf16[2,16,1024]{2,1,0:T(8,128)(2,1)S(1)} %fusion.27), channel_id=1, source_target_pairs={{0,2},{2,0},{4,6},{6,4},{8,10},{10,8},{12,14},{14,12},{1,3},{3,1},... | collective-permute-start | bytes 196616 | tf_op jit(solution)/shard_map/ppermute | solution.py:18
  70.5 5.2 %collective-permute-start.36 = (bf16[2,16,1024]{2,1,0:T(8,128)(2,1)S(1)}, bf16[2,16,1024]{2,1,0:T(8,128)(2,1)S(1)}, u32[]{:S(2)}, u32[]{:S(2)}) collective-permute-start(bf16[2,16,1024]{2,1,0:T(8,128)(2,1)S(1)} %fusion.29), channel_id=1, source_target_pairs={{0,2},{2,0},{4,6},{6,4},{8,10},{10,8},{12,14},{14,12},{1,3},{3,1},... | collective-permute-start | bytes 196616 | tf_op jit(solution)/shard_map/ppermute | solution.py:18
  71.8 5.6 %collective-permute-start.33 = (bf16[2,16,1024]{2,1,0:T(8,128)(2,1)S(1)}, bf16[2,16,1024]{2,1,0:T(8,128)(2,1)S(1)}, u32[]{:S(2)}, u32[]{:S(2)}) collective-permute-start(bf16[2,16,1024]{2,1,0:T(8,128)(2,1)S(1)} %fusion.28), channel_id=1, source_target_pairs={{0,4},{2,6},{4,0},{6,2},{8,12},{10,14},{12,8},{14,10},{1,5},{3,7},... | collective-permute-start | bytes 196616 | tf_op jit(solution)/shard_map/ppermute | solution.py:18
  72.5 6.3 %collective-permute-start.28 = (bf16[16,1024]{1,0:T(8,128)(2,1)S(1)}, bf16[16,1024]{1,0:T(8,128)(2,1)S(1)}, u32[]{:S(2)}, u32[]{:S(2)}) collective-permute-start(bf16[16,1024]{1,0:T(8,128)(2,1)S(1)} %fusion.34), channel_id=1, source_target_pairs={{0,8},{2,10},{4,12},{6,14},{8,0},{10,2},{12,4},{14,6},{1,9},{3,11}... | collective-permute-start | bytes 98312 | tf_op jit(solution)/shard_map/ppermute | solution.py:18
  74.3 5.3 %collective-permute-start.31 = (bf16[16,1024]{1,0:T(8,128)(2,1)S(1)}, bf16[16,1024]{1,0:T(8,128)(2,1)S(1)}, u32[]{:S(2)}, u32[]{:S(2)}) collective-permute-start(bf16[16,1024]{1,0:T(8,128)(2,1)S(1)} %fusion.35), channel_id=1, source_target_pairs={{0,8},{2,10},{4,12},{6,14},{8,0},{10,2},{12,4},{14,6},{1,9},{3,11}... | collective-permute-start | bytes 98312 | tf_op jit(solution)/shard_map/ppermute | solution.py:18
  75.7 4.9 %collective-permute-start.37 = (bf16[16,1024]{1,0:T(8,128)(2,1)S(1)}, bf16[16,1024]{1,0:T(8,128)(2,1)S(1)}, u32[]{:S(2)}, u32[]{:S(2)}) collective-permute-start(bf16[16,1024]{1,0:T(8,128)(2,1)S(1)} %fusion.37), channel_id=1, source_target_pairs={{0,8},{2,10},{4,12},{6,14},{8,0},{10,2},{12,4},{14,6},{1,9},{3,11}... | collective-permute-start | bytes 98312 | tf_op jit(solution)/shard_map/ppermute | solution.py:18
  77.5 5.2 %collective-permute-start.34 = (bf16[16,1024]{1,0:T(8,128)(2,1)S(1)}, bf16[16,1024]{1,0:T(8,128)(2,1)S(1)}, u32[]{:S(2)}, u32[]{:S(2)}) collective-permute-start(bf16[16,1024]{1,0:T(8,128)(2,1)S(1)} %fusion.36), channel_id=1, source_target_pairs={{0,8},{2,10},{4,12},{6,14},{8,0},{10,2},{12,4},{14,6},{1,9},{3,11}... | collective-permute-start | bytes 98312 | tf_op jit(solution)/shard_map/ppermute | solution.py:18

commit v25 on v23

--- a/solution.py
+++ b/solution.py
@@ -134,33 +134,33 @@
     )(start, slab)
 
 
-def matmul(left, right, exact=True):
-    if not exact:
+def split(value):
+    high = value.astype(jnp.bfloat16)
+    return high, (value - high.astype(jnp.float32)).astype(jnp.bfloat16)
+
+
+def matmul(left, right, exact=True, contract=0):
+    if exact:
+        (high, low), (other_high, other_low) = split(left), split(right)
+        left = jnp.concatenate([high, high, low], axis=1)
+        right = jnp.concatenate([other_high, other_low, other_high], axis=contract)
+    else:
         left, right = left.astype(jnp.bfloat16), right.astype(jnp.bfloat16)
     return lax.dot_general(
-        left,
-        right,
-        (((1,), (0,)), ((), ())),
-        precision=lax.Precision.HIGHEST if exact else None,
-        preferred_element_type=jnp.float32,
+        left, right, (((1,), (contract,)), ((), ())), preferred_element_type=jnp.float32
     )
 
 
-def matmul_t(left, right, exact=True):
-    if not exact:
-        left, right = left.astype(jnp.bfloat16), right.astype(jnp.bfloat16)
-    return lax.dot_general(
-        left,
-        right,
-        (((1,), (1,)), ((), ())),
-        precision=lax.Precision.HIGHEST if exact else None,
-        preferred_element_type=jnp.float32,
+def matmul_full(left, right):
+    return jnp.dot(
+        left, right, precision=lax.Precision.HIGHEST, preferred_element_type=jnp.float32
     )
 
 
-def gram_kernel(total_cols, mine_ref, other_ref, packed_ref):
+def gram_kernel(total_cols, mine_ref, other_ref, packed_ref, sketch_ref):
     sketch = (mine_ref[...] + other_ref[...]) / total_cols
-    gram = matmul(sketch.T, sketch)
+    sketch_ref[...] = sketch.T
+    gram = matmul_full(sketch_ref[...], sketch)
     half = gram.shape[0] // 2
     row = lax.broadcasted_iota(jnp.int32, (half, 2 * half), 0)
     col = lax.broadcasted_iota(jnp.int32, (half, 2 * half), 1)
@@ -188,9 +188,12 @@
     rows, width = mine.shape
     return pl.pallas_call(
         functools.partial(gram_kernel, total_cols),
-        out_shape=jax.ShapeDtypeStruct((width // 2 + 8, width), jnp.float32),
+        out_shape=[
+            jax.ShapeDtypeStruct((width // 2 + 8, width), jnp.float32),
+            jax.ShapeDtypeStruct((width, rows), jnp.float32),
+        ],
         in_specs=[pl.BlockSpec(memory_space=pltpu.VMEM)] * 2,
-        out_specs=pl.BlockSpec(memory_space=pltpu.VMEM),
+        out_specs=[pl.BlockSpec(memory_space=pltpu.VMEM)] * 2,
         compiler_params=pltpu.CompilerParams(vmem_limit_bytes=16 * 2**20),
         name="make_gram",
     )(mine, other)
@@ -202,7 +205,7 @@
 
 
 def basis_kernel(
-    total_cols, root_rows, gram_ref, mine_ref, other_ref, slab_ref,
+    root_rows, gram_ref, sketch_ref, slab_ref,
     basis_ref, *refs,
 ):
     products, (work_ref, inverse_ref, buffer, arrived) = refs[:-4], refs[-4:]
@@ -226,9 +229,11 @@
     inverse = unit - step + matmul(step, step, False)
     for update in range(1, UPDATES):
         exact = update >= LOOSE_UPDATES
-        error = matmul_t(matmul(inverse, scaled, exact), inverse, exact) - unit
+        error = matmul(matmul(inverse, scaled, exact), inverse, exact, 1) - unit
         step = error * half
-        inverse = inverse - matmul(step, inverse - matmul(step, inverse, exact), exact)
+        if update < UPDATES - 1:
+            step = step - matmul(step, step, exact)
+        inverse = inverse - matmul(step, inverse, exact)
     inverse_ref[...] = inverse * across
     far = jnp.sum(error * error)
 
@@ -253,12 +258,8 @@
         pivots = jnp.sum(jnp.where(on_diag, work_ref[...], 0.0), axis=1, keepdims=True)
         inverse_ref[...] = inverse_ref[...] * lax.rsqrt(pivots)
 
-    sketch = (mine_ref[...] + other_ref[...]) / total_cols
-    basis = matmul_t(sketch, inverse_ref[...]) * root_rows
-    basis_ref[...] = basis
-    high = basis.astype(jnp.bfloat16)
-    low = (basis - high.astype(jnp.float32)).astype(jnp.bfloat16)
-    pair = jnp.concatenate([high, low], axis=1).T
+    basis = matmul_full(inverse_ref[...], sketch_ref[...]) * root_rows
+    pair = jnp.concatenate(split(basis), axis=0)
     fetch.wait()
     for start in range(0, buffer.shape[1], TILE):
         both = lax.dot_general(
@@ -269,16 +270,17 @@
         )
         out, inner = divmod(start, products[0].shape[1])
         products[out][:, inner : inner + TILE] = both[:width] + both[width:]
-
-
-def make_basis(gram, mine, other, slab, total_cols, root_rows, chunks):
-    rows, width = mine.shape
+    basis_ref[...] = basis.T
+
+
+def make_basis(gram, sketch, slab, root_rows, chunks):
+    width, rows = sketch.shape
     cols = slab.shape[1]
     return pl.pallas_call(
-        functools.partial(basis_kernel, total_cols, root_rows),
+        functools.partial(basis_kernel, root_rows),
         out_shape=[jax.ShapeDtypeStruct((rows, width), jnp.float32)]
         + [jax.ShapeDtypeStruct((width, cols // chunks), jnp.float32)] * chunks,
-        in_specs=[pl.BlockSpec(memory_space=pltpu.VMEM)] * 3
+        in_specs=[pl.BlockSpec(memory_space=pltpu.VMEM)] * 2
         + [pl.BlockSpec(memory_space=pl.ANY)],
         out_specs=[pl.BlockSpec(memory_space=pltpu.VMEM)] * (1 + chunks),
         scratch_shapes=[
@@ -289,7 +291,7 @@
         ],
         compiler_params=pltpu.CompilerParams(vmem_limit_bytes=KERNEL_VMEM),
         name="make_basis",
-    )(gram, mine, other, slab)
+    )(gram, sketch, slab)
 
 
 def per_device(activations, start_sketch):
@@ -318,11 +320,8 @@
             preferred_element_type=jnp.float32,
         )
     other_sketch = swap(partial_sketch, "col", 1)
-    gram = row_sum(make_gram(partial_sketch, other_sketch, total_cols))
-    basis, *products = make_basis(
-        gram, partial_sketch, other_sketch, activations, total_cols, root_rows, CHUNKS
-    )
-
+    packed, sketch = make_gram(partial_sketch, other_sketch, total_cols)
+    basis, *products = make_basis(row_sum(packed), sketch, activations, root_rows, CHUNKS)
     pieces = [
         scatter_sum(product, "row", orders[c % 2]) / total_rows
         for c, product in enumerate(products)

time: 81.9 us -> 81.8 us (level)
  no operation moved by 1% of the time
where the time goes in v25:
time: 81.8 us; the launch traced here: 81.6 us
  starting transfers between devices  44.5 us (54%)
  waiting for transfers between devices  22.3 us (27%)
  Pallas kernels  8.67 us (11%)
  other arithmetic  2.12 us (3%)
  matrix products  1.77 us (2%)
  between operations  1.12 us (1%)
  local copies, waits for them, and re-layouts  1.05 us (1%)
    ppermute x34, starting transfers between devices, swap(): return lax.ppermute(value, axis, [(i, i ^ distance) for i in range(size)])  39.4 us
    ppermute x34, waiting for transfers between devices, swap(): return lax.ppermute(value, axis, [(i, i ^ distance) for i in range(size)])  19.6 us
    ppermute x4, starting transfers between devices, row_sum(): terms.append(lax.ppermute(value, ('row', 'col'), pairs))  5.1 us
    pallas_call x1, Pallas kernels, make_basis(): pl.pallas_call(functools.partial(basis_kernel, root_rows), out_shape=[jax...  4.1 us
    pallas_call x2, Pallas kernels, first_product(): pl.pallas_call(functools.partial(sketch_kernel, begin), out_shape=[jax.Sh...  4.07 us
    ppermute x4, waiting for transfers between devices, row_sum(): terms.append(lax.ppermute(value, ('row', 'col'), pairs))  2.67 us
    dot_general x4, matrix products, per_device(): lax.dot_general(activations[:, span], shared, (((1,), (1,)), ((), ())), p...  1.77 us
  transfers between devices with their start and end apart: 38, of which 19 were waited for; matrix products, arithmetic and copies ran while one was open for 3% of the time, Pallas kernels for 2%

profile of v25, /device:TPU:0, one launch (start us, length us, event | category | flops | bytes accessed | tf_op | source)
XLA Modules:
  0.0 81.6 jit_solution(5917887308849046841)
XLA Ops:
  0.7 0.9 %copy-done = bf16[512,128]{1,0:T(8,128)(2,1)S(1)} copy-done((bf16[512,128]{1,0:T(8,128)(2,1)S(1)}, bf16[512,128]{1,0:T(8,128)(2,1)}, u32[]{:S(2)}) %copy-start) | copy-done | bytes 131096
  1.6 2.1 %first_product.3 = (f32[128,1024]{1,0:T(8,128)S(1)}, f32[128,1024]{1,0:T(8,128)S(1)}) custom-call(bf16[512,128]{1,0:T(8,128)(2,1)S(1)} %copy-done, bf16[512,4096]{1,0:T(8,128)(2,1)} %slab_ref.5), custom_call_target="tpu_custom_call" | custom-call | flops 268435456 | bytes 2097152 | tf_op jit(solution)/shard_map/first_product/pallas_call | solution.py:117
  3.6 3.1 %collective-permute-start.15 = (bf16[128,512]{1,0:T(8,128)(2,1)S(1)}, bf16[128,512]{1,0:T(8,128)(2,1)S(1)}, u32[]{:S(2)}, u32[]{:S(2)}) collective-permute-start(bf16[128,512]{1,0:T(8,128)(2,1)S(1)} %select_convert_fusion.4), channel_id=1, source_target_pairs={{0,4},{2,6},{4,0},{6,2},{8,12},{10,14},{12,8},{14,10},{1,5},{3,7},... | collective-permute-start | bytes 393224 | tf_op jit(solution)/shard_map/ppermute | solution.py:18
  6.8 1.6 %collective-permute-start.10 = (bf16[128,512]{1,0:T(8,128)(2,1)S(1)}, bf16[128,512]{1,0:T(8,128)(2,1)S(1)}, u32[]{:S(2)}, u32[]{:S(2)}) collective-permute-start(bf16[128,512]{1,0:T(8,128)(2,1)S(1)} %select_convert_fusion.5), channel_id=1, source_target_pairs={{0,2},{2,0},{4,6},{6,4},{8,10},{10,8},{12,14},{14,12},{1,3},{3,1},... | collective-permute-start | bytes 393224 | tf_op jit(solution)/shard_map/ppermute | solution.py:18
  8.3 2.0 %first_product.2 = (f32[128,1024]{1,0:T(8,128)S(1)}, f32[128,1024]{1,0:T(8,128)S(1)}) custom-call(bf16[512,128]{1,0:T(8,128)(2,1)S(1)} %copy-done.1, bf16[512,4096]{1,0:T(8,128)(2,1)} %slab_ref.5), custom_call_target="tpu_custom_call" | custom-call | flops 268435456 | bytes 2097152 | tf_op jit(solution)/shard_map/first_product/pallas_call | solution.py:117
  11.2 2.0 %collective-permute-start.16 = (bf16[128,256]{1,0:T(8,128)(2,1)S(1)}, bf16[128,256]{1,0:T(8,128)(2,1)S(1)}, u32[]{:S(2)}, u32[]{:S(2)}) collective-permute-start(bf16[128,256]{1,0:T(8,128)(2,1)S(1)} %select_convert_fusion.12), channel_id=1, source_target_pairs={{0,2},{2,0},{4,6},{6,4},{8,10},{10,8},{12,14},{14,12},{1,3},{3,1},... | collective-permute-start | bytes 196616 | tf_op jit(solution)/shard_map/ppermute | solution.py:18
  13.3 1.6 %collective-permute-start.11 = (bf16[128,256]{1,0:T(8,128)(2,1)S(1)}, bf16[128,256]{1,0:T(8,128)(2,1)S(1)}, u32[]{:S(2)}, u32[]{:S(2)}) collective-permute-start(bf16[128,256]{1,0:T(8,128)(2,1)S(1)} %select_convert_fusion.13), channel_id=1, source_target_pairs={{0,4},{2,6},{4,0},{6,2},{8,12},{10,14},{12,8},{14,10},{1,5},{3,7},... | collective-permute-start | bytes 196616 | tf_op jit(solution)/shard_map/ppermute | solution.py:18
  14.9 1.2 %collective-permute-done.5 = bf16[128,512]{1,0:T(8,128)(2,1)S(1)} collective-permute-done((bf16[128,512]{1,0:T(8,128)(2,1)S(1)}, bf16[128,512]{1,0:T(8,128)(2,1)S(1)}, u32[]{:S(2)}, u32[]{:S(2)}) %collective-permute-start.5) | collective-permute-done | bytes 131104 | tf_op jit(solution)/shard_map/ppermute | solution.py:18
  16.2 0.6 collective-permute-start.6
  16.9 1.6 %collective-permute-start.1 = (bf16[128,256]{1,0:T(8,128)(2,1)S(1)}, bf16[128,256]{1,0:T(8,128)(2,1)S(1)}, u32[]{:S(2)}, u32[]{:S(2)}) collective-permute-start(bf16[128,256]{1,0:T(8,128)(2,1)S(1)} %select_convert_fusion.15), channel_id=1, source_target_pairs={{0,4},{2,6},{4,0},{6,2},{8,12},{10,14},{12,8},{14,10},{1,5},{3,7},... | collective-permute-start | bytes 196616 | tf_op jit(solution)/shard_map/ppermute | solution.py:18
  18.6 2.7 %collective-permute-start.17 = (bf16[128,256]{1,0:T(8,128)(2,1)S(1)}, bf16[128,256]{1,0:T(8,128)(2,1)S(1)}, u32[]{:S(2)}, u32[]{:S(2)}) collective-permute-start(bf16[128,256]{1,0:T(8,128)(2,1)S(1)} %fusion.41), channel_id=1, source_target_pairs={{0,8},{2,10},{4,12},{6,14},{8,0},{10,2},{12,4},{14,6},{1,9},{3,11}... | collective-permute-start | bytes 196616 | tf_op jit(solution)/shard_map/ppermute | solution.py:18
  21.7 2.7 %collective-permute-start.7 = (bf16[128,256]{1,0:T(8,128)(2,1)S(1)}, bf16[128,256]{1,0:T(8,128)(2,1)S(1)}, u32[]{:S(2)}, u32[]{:S(2)}) collective-permute-start(bf16[128,256]{1,0:T(8,128)(2,1)S(1)} %fusion.39), channel_id=1, source_target_pairs={{0,8},{2,10},{4,12},{6,14},{8,0},{10,2},{12,4},{14,6},{1,9},{3,11}... | collective-permute-start | bytes 196616 | tf_op jit(solution)/shard_map/ppermute | solution.py:18
  24.8 2.4 %collective-permute-done.17 = bf16[128,256]{1,0:T(8,128)(2,1)S(1)} collective-permute-done((bf16[128,256]{1,0:T(8,128)(2,1)S(1)}, bf16[128,256]{1,0:T(8,128)(2,1)S(1)}, u32[]{:S(2)}, u32[]{:S(2)}) %collective-permute-start.17) | collective-permute-done | bytes 65568 | tf_op jit(solution)/shard_map/ppermute | solution.py:18
  27.2 2.7 %collective-permute-done.12 = bf16[128,256]{1,0:T(8,128)(2,1)S(1)} collective-permute-done((bf16[128,256]{1,0:T(8,128)(2,1)S(1)}, bf16[128,256]{1,0:T(8,128)(2,1)S(1)}, u32[]{:S(2)}, u32[]{:S(2)}) %collective-permute-start.12) | collective-permute-done | bytes 65568 | tf_op jit(solution)/shard_map/ppermute | solution.py:18
  30.1 0.6 collective-permute-done.7
  30.7 0.6 collective-permute-start.8
  31.4 0.9 %collective-permute-start.3 = (bf16[128,256]{1,0:T(8,128)(2,1)S(1)}, bf16[128,256]{1,0:T(8,128)(2,1)S(1)}, u32[]{:S(2)}, u32[]{:S(2)}) collective-permute-start(bf16[128,256]{1,0:T(8,128)(2,1)S(1)} %multiply_convert_fusion.3), channel_id=1, source_target_pairs={{0,4},{2,6},{4,0},{6,2},{8,12},{10,14},{12,8},{14,10},{1,5},{3,7},... | collective-permute-start | bytes 196616 | tf_op jit(solution)/shard_map/ppermute | solution.py:18
  32.4 1.2 %collective-permute-start.19 = (bf16[128,512]{1,0:T(8,128)(2,1)S(1)}, bf16[128,512]{1,0:T(8,128)(2,1)S(1)}, u32[]{:S(2)}, u32[]{:S(2)}) collective-permute-start(bf16[128,512]{1,0:T(8,128)(2,1)S(1)} %pad_maximum_fusion.4), channel_id=1, source_target_pairs={{0,4},{2,6},{4,0},{6,2},{8,12},{10,14},{12,8},{14,10},{1,5},{3,7},... | collective-permute-start | bytes 393224 | tf_op jit(solution)/shard_map/ppermute | solution.py:18
  33.6 1.4 %collective-permute-done.13 = bf16[128,256]{1,0:T(8,128)(2,1)S(1)} collective-permute-done((bf16[128,256]{1,0:T(8,128)(2,1)S(1)}, bf16[128,256]{1,0:T(8,128)(2,1)S(1)}, u32[]{:S(2)}, u32[]{:S(2)}) %collective-permute-start.13) | collective-permute-done | bytes 65568 | tf_op jit(solution)/shard_map/ppermute | solution.py:18
  35.6 1.4 %collective-permute-start.9 = (bf16[128,512]{1,0:T(8,128)(2,1)S(1)}, bf16[128,512]{1,0:T(8,128)(2,1)S(1)}, u32[]{:S(2)}, u32[]{:S(2)}) collective-permute-start(bf16[128,512]{1,0:T(8,128)(2,1)S(1)} %pad_maximum_fusion.2), channel_id=1, source_target_pairs={{0,4},{2,6},{4,0},{6,2},{8,12},{10,14},{12,8},{14,10},{1,5},{3,7},... | collective-permute-start | bytes 393224 | tf_op jit(solution)/shard_map/ppermute | solution.py:18
  37.1 0.9 %collective-permute-start.4 = (bf16[128,512]{1,0:T(8,128)(2,1)S(1)}, bf16[128,512]{1,0:T(8,128)(2,1)S(1)}, u32[]{:S(2)}, u32[]{:S(2)}) collective-permute-start(bf16[128,512]{1,0:T(8,128)(2,1)S(1)} %pad_maximum_fusion.1), channel_id=1, source_target_pairs={{0,2},{2,0},{4,6},{6,4},{8,10},{10,8},{12,14},{14,12},{1,3},{3,1},... | collective-permute-start | bytes 393224 | tf_op jit(solution)/shard_map/ppermute | solution.py:18
  38.0 1.1 %collective-permute-done.19 = bf16[128,512]{1,0:T(8,128)(2,1)S(1)} collective-permute-done((bf16[128,512]{1,0:T(8,128)(2,1)S(1)}, bf16[128,512]{1,0:T(8,128)(2,1)S(1)}, u32[]{:S(2)}, u32[]{:S(2)}) %collective-permute-start.19) | collective-permute-done | bytes 131104 | tf_op jit(solution)/shard_map/ppermute | solution.py:18
  41.2 1.0 %collective-permute-done.4 = bf16[128,512]{1,0:T(8,128)(2,1)S(1)} collective-permute-done((bf16[128,512]{1,0:T(8,128)(2,1)S(1)}, bf16[128,512]{1,0:T(8,128)(2,1)S(1)}, u32[]{:S(2)}, u32[]{:S(2)}) %collective-permute-start.4) | collective-permute-done | bytes 131104 | tf_op jit(solution)/shard_map/ppermute | solution.py:18
  42.7 1.5 %collective-permute-done.20.other_ref = f32[512,128]{1,0:T(8,128)S(1)} collective-permute-done((f32[512,128]{1,0:T(8,128)S(1)}, f32[512,128]{1,0:T(8,128)S(1)}, u32[]{:S(2)}, u32[]{:S(2)}) %collective-permute-start.20) | collective-permute-done | bytes 262176 | tf_op jit(solution)/shard_map/ppermute | solution.py:18
  44.7 2.3 %collective-permute-start.24 = (f32[72,128]{1,0:T(8,128)S(1)}, f32[72,128]{1,0:T(8,128)S(1)}, u32[]{:S(2)}, u32[]{:S(2)}) collective-permute-start(f32[72,128]{1,0:T(8,128)S(1)} %get-tuple-element.17), channel_id=1, source_target_pairs={{0,10},{1,15},{2,8},{3,13},{4,14},{5,11},{6,12},{7,9},{8,2},{9,7},... | collective-permute-start | bytes 110600 | tf_op jit(solution)/shard_map/ppermute | solution.py:36
  47.0 0.9 %collective-permute-start.23 = (f32[72,128]{1,0:T(8,128)S(1)}, f32[72,128]{1,0:T(8,128)S(1)}, u32[]{:S(2)}, u32[]{:S(2)}) collective-permute-start(f32[72,128]{1,0:T(8,128)S(1)} %get-tuple-element.17), channel_id=1, source_target_pairs={{0,8},{1,13},{2,10},{3,15},{4,12},{5,9},{6,14},{7,11},{8,0},{9,5},... | collective-permute-start | bytes 110600 | tf_op jit(solution)/shard_map/ppermute | solution.py:36
  48.0 1.2 %collective-permute-start.22 = (f32[72,128]{1,0:T(8,128)S(1)}, f32[72,128]{1,0:T(8,128)S(1)}, u32[]{:S(2)}, u32[]{:S(2)}) collective-permute-start(f32[72,128]{1,0:T(8,128)S(1)} %get-tuple-element.17), channel_id=1, source_target_pairs={{0,2},{1,7},{2,0},{3,5},{4,6},{5,3},{6,4},{7,1},{8,10},{9,15},{10,... | collective-permute-start | bytes 110600 | tf_op jit(solution)/shard_map/ppermute | solution.py:36
  49.2 0.7 collective-permute-start.21
  49.9 1.5 %collective-permute-done.24 = f32[72,128]{1,0:T(8,128)S(1)} collective-permute-done((f32[72,128]{1,0:T(8,128)S(1)}, f32[72,128]{1,0:T(8,128)S(1)}, u32[]{:S(2)}, u32[]{:S(2)}) %collective-permute-start.24) | collective-permute-done | bytes 36896 | tf_op jit(solution)/shard_map/ppermute | solution.py:36
  51.4 1.2 %collective-permute-done.23 = f32[72,128]{1,0:T(8,128)S(1)} collective-permute-done((f32[72,128]{1,0:T(8,128)S(1)}, f32[72,128]{1,0:T(8,128)S(1)}, u32[]{:S(2)}, u32[]{:S(2)}) %collective-permute-start.23) | collective-permute-done | bytes 36896 | tf_op jit(solution)/shard_map/ppermute | solution.py:36
  52.5 1.3 %collective-permute-start.25 = (f32[72,128]{1,0:T(8,128)S(1)}, f32[72,128]{1,0:T(8,128)S(1)}, u32[]{:S(2)}, u32[]{:S(2)}) collective-permute-start(f32[72,128]{1,0:T(8,128)S(1)} %add_add_fusion), channel_id=1, source_target_pairs={{0,1},{1,0},{2,3},{3,2},{4,5},{5,4},{6,7},{7,6},{8,9},{9,8},{10,11... | collective-permute-start | bytes 110600 | tf_op jit(solution)/shard_map/ppermute | solution.py:18
  53.9 0.9 %collective-permute-done.25 = f32[72,128]{1,0:T(8,128)S(1)} collective-permute-done((f32[72,128]{1,0:T(8,128)S(1)}, f32[72,128]{1,0:T(8,128)S(1)}, u32[]{:S(2)}, u32[]{:S(2)}) %collective-permute-start.25) | collective-permute-done | bytes 36896 | tf_op jit(solution)/shard_map/ppermute | solution.py:18
  54.8 4.1 %make_basis.1 = (f32[512,128]{1,0:T(8,128)}, f32[128,1024]{1,0:T(8,128)S(1)}, f32[128,1024]{1,0:T(8,128)S(1)}, f32[128,1024]{1,0:T(8,128)S(1)}, f32[128,1024]{1,0:T(8,128)S(1)}) custom-call(f32[72,128]{1,0:T(8,128)S(1)} %add.116.gram_ref, f32[128,512]{1,0:T(8,128)S(1)} %get-tuple-element.18.sketch_ref, bf16[512,4096]{1,0:T(8,128)(2,1)} %slab_ref.5), custom_call_target="tpu_custom_call" | custom-call | tf_op jit(solution)/shard_map/make_basis/pallas_call | solution.py:279
  59.0 0.9 %collective-permute-start.26 = (bf16[2,2,16,1024]{3,2,0,1:T(8,128)(2,1)S(1)}, bf16[2,2,16,1024]{3,2,0,1:T(8,128)(2,1)S(1)}, u32[]{:S(2)}, u32[]{:S(2)}) collective-permute-start(bf16[2,2,16,1024]{3,2,0,1:T(8,128)(2,1)S(1)} %fusion.22), channel_id=1, source_target_pairs={{0,2},{2,0},{4,6},{6,4},{8,10},{10,8},{12,14},{14,12},{1,3},{3,1},... | collective-permute-start | bytes 393224 | tf_op jit(solution)/shard_map/ppermute | solution.py:18
  59.9 1.8 %collective-permute-start.29 = (bf16[2,2,16,1024]{3,2,0,1:T(8,128)(2,1)S(1)}, bf16[2,2,16,1024]{3,2,0,1:T(8,128)(2,1)S(1)}, u32[]{:S(2)}, u32[]{:S(2)}) collective-permute-start(bf16[2,2,16,1024]{3,2,0,1:T(8,128)(2,1)S(1)} %fusion.23), channel_id=1, source_target_pairs={{0,4},{2,6},{4,0},{6,2},{8,12},{10,14},{12,8},{14,10},{1,5},{3,7},... | collective-permute-start | bytes 393224 | tf_op jit(solution)/shard_map/ppermute | solution.py:18
  61.8 1.3 %collective-permute-start.32 = (bf16[2,2,16,1024]{3,2,0,1:T(8,128)(2,1)S(1)}, bf16[2,2,16,1024]{3,2,0,1:T(8,128)(2,1)S(1)}, u32[]{:S(2)}, u32[]{:S(2)}) collective-permute-start(bf16[2,2,16,1024]{3,2,0,1:T(8,128)(2,1)S(1)} %fusion.24), channel_id=1, source_target_pairs={{0,2},{2,0},{4,6},{6,4},{8,10},{10,8},{12,14},{14,12},{1,3},{3,1},... | collective-permute-start | bytes 393224 | tf_op jit(solution)/shard_map/ppermute | solution.py:18
  63.5 1.8 %collective-permute-done.26 = bf16[2,2,16,1024]{3,2,0,1:T(8,128)(2,1)S(1)} collective-permute-done((bf16[2,2,16,1024]{3,2,0,1:T(8,128)(2,1)S(1)}, bf16[2,2,16,1024]{3,2,0,1:T(8,128)(2,1)S(1)}, u32[]{:S(2)}, u32[]{:S(2)}) %collective-permute-start.26) | collective-permute-done | bytes 131104 | tf_op jit(solution)/shard_map/ppermute | solution.py:18
  65.3 1.9 %collective-permute-start.27 = (bf16[2,16,1024]{2,1,0:T(8,128)(2,1)S(1)}, bf16[2,16,1024]{2,1,0:T(8,128)(2,1)S(1)}, u32[]{:S(2)}, u32[]{:S(2)}) collective-permute-start(bf16[2,16,1024]{2,1,0:T(8,128)(2,1)S(1)} %fusion.26), channel_id=1, source_target_pairs={{0,4},{2,6},{4,0},{6,2},{8,12},{10,14},{12,8},{14,10},{1,5},{3,7},... | collective-permute-start | bytes 196616 | tf_op jit(solution)/shard_map/ppermute | solution.py:18
  67.3 0.9 %collective-permute-start.30 = (bf16[2,16,1024]{2,1,0:T(8,128)(2,1)S(1)}, bf16[2,16,1024]{2,1,0:T(8,128)(2,1)S(1)}, u32[]{:S(2)}, u32[]{:S(2)}) collective-permute-start(bf16[2,16,1024]{2,1,0:T(8,128)(2,1)S(1)} %fusion.27), channel_id=1, source_target_pairs={{0,2},{2,0},{4,6},{6,4},{8,10},{10,8},{12,14},{14,12},{1,3},{3,1},... | collective-permute-start | bytes 196616 | tf_op jit(solution)/shard_map/ppermute | solution.py:18
  68.2 1.3 %collective-permute-start.33 = (bf16[2,16,1024]{2,1,0:T(8,128)(2,1)S(1)}, bf16[2,16,1024]{2,1,0:T(8,128)(2,1)S(1)}, u32[]{:S(2)}, u32[]{:S(2)}) collective-permute-start(bf16[2,16,1024]{2,1,0:T(8,128)(2,1)S(1)} %fusion.28), channel_id=1, source_target_pairs={{0,4},{2,6},{4,0},{6,2},{8,12},{10,14},{12,8},{14,10},{1,5},{3,7},... | collective-permute-start | bytes 196616 | tf_op jit(solution)/shard_map/ppermute | solution.py:18
  69.6 0.9 %collective-permute-start.36 = (bf16[2,16,1024]{2,1,0:T(8,128)(2,1)S(1)}, bf16[2,16,1024]{2,1,0:T(8,128)(2,1)S(1)}, u32[]{:S(2)}, u32[]{:S(2)}) collective-permute-start(bf16[2,16,1024]{2,1,0:T(8,128)(2,1)S(1)} %fusion.29), channel_id=1, source_target_pairs={{0,2},{2,0},{4,6},{6,4},{8,10},{10,8},{12,14},{14,12},{1,3},{3,1},... | collective-permute-start | bytes 196616 | tf_op jit(solution)/shard_map/ppermute | solution.py:18
  70.5 1.9 %collective-permute-start.28 = (bf16[16,1024]{1,0:T(8,128)(2,1)S(1)}, bf16[16,1024]{1,0:T(8,128)(2,1)S(1)}, u32[]{:S(2)}, u32[]{:S(2)}) collective-permute-start(bf16[16,1024]{1,0:T(8,128)(2,1)S(1)} %fusion.34), channel_id=1, source_target_pairs={{0,8},{2,10},{4,12},{6,14},{8,0},{10,2},{12,4},{14,6},{1,9},{3,11}... | collective-permute-start | bytes 98312 | tf_op jit(solution)/shard_map/ppermute | solution.py:18
  72.4 1.2 %collective-permute-start.31 = (bf16[16,1024]{1,0:T(8,128)(2,1)S(1)}, bf16[16,1024]{1,0:T(8,128)(2,1)S(1)}, u32[]{:S(2)}, u32[]{:S(2)}) collective-permute-start(bf16[16,1024]{1,0:T(8,128)(2,1)S(1)} %fusion.35), channel_id=1, source_target_pairs={{0,8},{2,10},{4,12},{6,14},{8,0},{10,2},{12,4},{14,6},{1,9},{3,11}... | collective-permute-start | bytes 98312 | tf_op jit(solution)/shard_map/ppermute | solution.py:18
  73.7 1.8 %collective-permute-start.34 = (bf16[16,1024]{1,0:T(8,128)(2,1)S(1)}, bf16[16,1024]{1,0:T(8,128)(2,1)S(1)}, u32[]{:S(2)}, u32[]{:S(2)}) collective-permute-start(bf16[16,1024]{1,0:T(8,128)(2,1)S(1)} %fusion.36), channel_id=1, source_target_pairs={{0,8},{2,10},{4,12},{6,14},{8,0},{10,2},{12,4},{14,6},{1,9},{3,11}... | collective-permute-start | bytes 98312 | tf_op jit(solution)/shard_map/ppermute | solution.py:18
  75.6 1.2 %collective-permute-start.37 = (bf16[16,1024]{1,0:T(8,128)(2,1)S(1)}, bf16[16,1024]{1,0:T(8,128)(2,1)S(1)}, u32[]{:S(2)}, u32[]{:S(2)}) collective-permute-start(bf16[16,1024]{1,0:T(8,128)(2,1)S(1)} %fusion.37), channel_id=1, source_target_pairs={{0,8},{2,10},{4,12},{6,14},{8,0},{10,2},{12,4},{14,6},{1,9},{3,11}... | collective-permute-start | bytes 98312 | tf_op jit(solution)/shard_map/ppermute | solution.py:18
  76.8 1.3 %collective-permute-done.31 = bf16[16,1024]{1,0:T(8,128)(2,1)S(1)} collective-permute-done((bf16[16,1024]{1,0:T(8,128)(2,1)S(1)}, bf16[16,1024]{1,0:T(8,128)(2,1)S(1)}, u32[]{:S(2)}, u32[]{:S(2)}) %collective-permute-start.31) | collective-permute-done | bytes 32800 | tf_op jit(solution)/shard_map/ppermute | solution.py:18
  78.7 2.1 %collective-permute-done.37 = bf16[16,1024]{1,0:T(8,128)(2,1)S(1)} collective-permute-done((bf16[16,1024]{1,0:T(8,128)(2,1)S(1)}, bf16[16,1024]{1,0:T(8,128)(2,1)S(1)}, u32[]{:S(2)}, u32[]{:S(2)}) %collective-permute-start.37) | collective-permute-done | bytes 32800 | tf_op jit(solution)/shard_map/ppermute | solution.py:18
  80.8 0.7 pad_maximum_fusion
  (105 shorter events, 7.7 us)
Async XLA Ops:
  0.6 0.9 %copy-start = (bf16[512,128]{1,0:T(8,128)(2,1)S(1)}, bf16[512,128]{1,0:T(8,128)(2,1)}, u32[]{:S(2)}) copy-start(bf16[512,128]{1,0:T(8,128)(2,1)} %start_ref.3) | copy-start | bytes 393220
  1.6 6.8 %copy-start.1 = (bf16[512,128]{1,0:T(8,128)(2,1)S(1)}, bf16[512,128]{1,0:T(8,128)(2,1)}, u32[]{:S(2)}) copy-start(bf16[512,128]{1,0:T(8,128)(2,1)} %start_ref.3) | copy-start | bytes 393220
  3.6 7.5 %collective-permute-start.15 = (bf16[128,512]{1,0:T(8,128)(2,1)S(1)}, bf16[128,512]{1,0:T(8,128)(2,1)S(1)}, u32[]{:S(2)}, u32[]{:S(2)}) collective-permute-start(bf16[128,512]{1,0:T(8,128)(2,1)S(1)} %select_convert_fusion.4), channel_id=1, source_target_pairs={{0,4},{2,6},{4,0},{6,2},{8,12},{10,14},{12,8},{14,10},{1,5},{3,7},... | collective-permute-start | bytes 393224 | tf_op jit(solution)/shard_map/ppermute | solution.py:18
  6.8 6.4 %collective-permute-start.10 = (bf16[128,512]{1,0:T(8,128)(2,1)S(1)}, bf16[128,512]{1,0:T(8,128)(2,1)S(1)}, u32[]{:S(2)}, u32[]{:S(2)}) collective-permute-start(bf16[128,512]{1,0:T(8,128)(2,1)S(1)} %select_convert_fusion.5), channel_id=1, source_target_pairs={{0,2},{2,0},{4,6},{6,4},{8,10},{10,8},{12,14},{14,12},{1,3},{3,1},... | collective-permute-start | bytes 393224 | tf_op jit(solution)/shard_map/ppermute | solution.py:18
  10.4 5.7 %collective-permute-start.5 = (bf16[128,512]{1,0:T(8,128)(2,1)S(1)}, bf16[128,512]{1,0:T(8,128)(2,1)S(1)}, u32[]{:S(2)}, u32[]{:S(2)}) collective-permute-start(bf16[128,512]{1,0:T(8,128)(2,1)S(1)} %select_convert_fusion.6), channel_id=1, source_target_pairs={{0,4},{2,6},{4,0},{6,2},{8,12},{10,14},{12,8},{14,10},{1,5},{3,7},... | collective-permute-start | bytes 393224 | tf_op jit(solution)/shard_map/ppermute | solution.py:18
  10.9 5.9 %collective-permute-start = (bf16[128,512]{1,0:T(8,128)(2,1)S(1)}, bf16[128,512]{1,0:T(8,128)(2,1)S(1)}, u32[]{:S(2)}, u32[]{:S(2)}) collective-permute-start(bf16[128,512]{1,0:T(8,128)(2,1)S(1)} %select_convert_fusion.7), channel_id=1, source_target_pairs={{0,2},{2,0},{4,6},{6,4},{8,10},{10,8},{12,14},{14,12},{1,3},{3,1},... | collective-permute-start | bytes 393224 | tf_op jit(solution)/shard_map/ppermute | solution.py:18
  11.2 7.3 %collective-permute-start.16 = (bf16[128,256]{1,0:T(8,128)(2,1)S(1)}, bf16[128,256]{1,0:T(8,128)(2,1)S(1)}, u32[]{:S(2)}, u32[]{:S(2)}) collective-permute-start(bf16[128,256]{1,0:T(8,128)(2,1)S(1)} %select_convert_fusion.12), channel_id=1, source_target_pairs={{0,2},{2,0},{4,6},{6,4},{8,10},{10,8},{12,14},{14,12},{1,3},{3,1},... | collective-permute-start | bytes 196616 | tf_op jit(solution)/shard_map/ppermute | solution.py:18
  13.2 25.9 %copy-start.2 = (bf16[512,4096]{1,0:T(8,128)(2,1)S(1)}, bf16[512,4096]{1,0:T(8,128)(2,1)}, u32[]{:S(2)}) copy-start(bf16[512,4096]{1,0:T(8,128)(2,1)} %slab_ref.5) | copy-start | bytes 12582916
  13.3 8.0 %collective-permute-start.11 = (bf16[128,256]{1,0:T(8,128)(2,1)S(1)}, bf16[128,256]{1,0:T(8,128)(2,1)S(1)}, u32[]{:S(2)}, u32[]{:S(2)}) collective-permute-start(bf16[128,256]{1,0:T(8,128)(2,1)S(1)} %select_convert_fusion.13), channel_id=1, source_target_pairs={{0,4},{2,6},{4,0},{6,2},{8,12},{10,14},{12,8},{14,10},{1,5},{3,7},... | collective-permute-start | bytes 196616 | tf_op jit(solution)/shard_map/ppermute | solution.py:18
  16.2 5.4 %collective-permute-start.6 = (bf16[128,256]{1,0:T(8,128)(2,1)S(1)}, bf16[128,256]{1,0:T(8,128)(2,1)S(1)}, u32[]{:S(2)}, u32[]{:S(2)}) collective-permute-start(bf16[128,256]{1,0:T(8,128)(2,1)S(1)} %select_convert_fusion.14), channel_id=1, source_target_pairs={{0,2},{2,0},{4,6},{6,4},{8,10},{10,8},{12,14},{14,12},{1,3},{3,1},... | collective-permute-start | bytes 196616 | tf_op jit(solution)/shard_map/ppermute | solution.py:18
  16.9 7.4 %collective-permute-start.1 = (bf16[128,256]{1,0:T(8,128)(2,1)S(1)}, bf16[128,256]{1,0:T(8,128)(2,1)S(1)}, u32[]{:S(2)}, u32[]{:S(2)}) collective-permute-start(bf16[128,256]{1,0:T(8,128)(2,1)S(1)} %select_convert_fusion.15), channel_id=1, source_target_pairs={{0,4},{2,6},{4,0},{6,2},{8,12},{10,14},{12,8},{14,10},{1,5},{3,7},... | collective-permute-start | bytes 196616 | tf_op jit(solution)/shard_map/ppermute | solution.py:18
  18.6 8.6 %collective-permute-start.17 = (bf16[128,256]{1,0:T(8,128)(2,1)S(1)}, bf16[128,256]{1,0:T(8,128)(2,1)S(1)}, u32[]{:S(2)}, u32[]{:S(2)}) collective-permute-start(bf16[128,256]{1,0:T(8,128)(2,1)S(1)} %fusion.41), channel_id=1, source_target_pairs={{0,8},{2,10},{4,12},{6,14},{8,0},{10,2},{12,4},{14,6},{1,9},{3,11}... | collective-permute-start | bytes 196616 | tf_op jit(solution)/shard_map/ppermute | solution.py:18
  21.2 8.7 %collective-permute-start.12 = (bf16[128,256]{1,0:T(8,128)(2,1)S(1)}, bf16[128,256]{1,0:T(8,128)(2,1)S(1)}, u32[]{:S(2)}, u32[]{:S(2)}) collective-permute-start(bf16[128,256]{1,0:T(8,128)(2,1)S(1)} %fusion.40), channel_id=1, source_target_pairs={{0,8},{2,10},{4,12},{6,14},{8,0},{10,2},{12,4},{14,6},{1,9},{3,11}... | collective-permute-start | bytes 196616 | tf_op jit(solution)/shard_map/ppermute | solution.py:18
  21.7 9.0 %collective-permute-start.7 = (bf16[128,256]{1,0:T(8,128)(2,1)S(1)}, bf16[128,256]{1,0:T(8,128)(2,1)S(1)}, u32[]{:S(2)}, u32[]{:S(2)}) collective-permute-start(bf16[128,256]{1,0:T(8,128)(2,1)S(1)} %fusion.39), channel_id=1, source_target_pairs={{0,8},{2,10},{4,12},{6,14},{8,0},{10,2},{12,4},{14,6},{1,9},{3,11}... | collective-permute-start | bytes 196616 | tf_op jit(solution)/shard_map/ppermute | solution.py:18
  24.4 7.0 %collective-permute-start.2 = (bf16[128,256]{1,0:T(8,128)(2,1)S(1)}, bf16[128,256]{1,0:T(8,128)(2,1)S(1)}, u32[]{:S(2)}, u32[]{:S(2)}) collective-permute-start(bf16[128,256]{1,0:T(8,128)(2,1)S(1)} %fusion.38), channel_id=1, source_target_pairs={{0,8},{2,10},{4,12},{6,14},{8,0},{10,2},{12,4},{14,6},{1,9},{3,11}... | collective-permute-start | bytes 196616 | tf_op jit(solution)/shard_map/ppermute | solution.py:18
  27.2 5.2 %collective-permute-start.18 = (bf16[128,256]{1,0:T(8,128)(2,1)S(1)}, bf16[128,256]{1,0:T(8,128)(2,1)S(1)}, u32[]{:S(2)}, u32[]{:S(2)}) collective-permute-start(bf16[128,256]{1,0:T(8,128)(2,1)S(1)} %multiply_convert_fusion), channel_id=1, source_target_pairs={{0,2},{2,0},{4,6},{6,4},{8,10},{10,8},{12,14},{14,12},{1,3},{3,1},... | collective-permute-start | bytes 196616 | tf_op jit(solution)/shard_map/ppermute | solution.py:18
  30.0 5.0 %collective-permute-start.13 = (bf16[128,256]{1,0:T(8,128)(2,1)S(1)}, bf16[128,256]{1,0:T(8,128)(2,1)S(1)}, u32[]{:S(2)}, u32[]{:S(2)}) collective-permute-start(bf16[128,256]{1,0:T(8,128)(2,1)S(1)} %multiply_convert_fusion.1), channel_id=1, source_target_pairs={{0,4},{2,6},{4,0},{6,2},{8,12},{10,14},{12,8},{14,10},{1,5},{3,7},... | collective-permute-start | bytes 196616 | tf_op jit(solution)/shard_map/ppermute | solution.py:18
  30.7 4.9 %collective-permute-start.8 = (bf16[128,256]{1,0:T(8,128)(2,1)S(1)}, bf16[128,256]{1,0:T(8,128)(2,1)S(1)}, u32[]{:S(2)}, u32[]{:S(2)}) collective-permute-start(bf16[128,256]{1,0:T(8,128)(2,1)S(1)} %multiply_convert_fusion.2), channel_id=1, source_target_pairs={{0,2},{2,0},{4,6},{6,4},{8,10},{10,8},{12,14},{14,12},{1,3},{3,1},... | collective-permute-start | bytes 196616 | tf_op jit(solution)/shard_map/ppermute | solution.py:18
  31.4 5.6 %collective-permute-start.3 = (bf16[128,256]{1,0:T(8,128)(2,1)S(1)}, bf16[128,256]{1,0:T(8,128)(2,1)S(1)}, u32[]{:S(2)}, u32[]{:S(2)}) collective-permute-start(bf16[128,256]{1,0:T(8,128)(2,1)S(1)} %multiply_convert_fusion.3), channel_id=1, source_target_pairs={{0,4},{2,6},{4,0},{6,2},{8,12},{10,14},{12,8},{14,10},{1,5},{3,7},... | collective-permute-start | bytes 196616 | tf_op jit(solution)/shard_map/ppermute | solution.py:18
  32.4 6.8 %collective-permute-start.19 = (bf16[128,512]{1,0:T(8,128)(2,1)S(1)}, bf16[128,512]{1,0:T(8,128)(2,1)S(1)}, u32[]{:S(2)}, u32[]{:S(2)}) collective-permute-start(bf16[128,512]{1,0:T(8,128)(2,1)S(1)} %pad_maximum_fusion.4), channel_id=1, source_target_pairs={{0,4},{2,6},{4,0},{6,2},{8,12},{10,14},{12,8},{14,10},{1,5},{3,7},... | collective-permute-start | bytes 393224 | tf_op jit(solution)/shard_map/ppermute | solution.py:18
  35.0 5.0 %collective-permute-start.14 = (bf16[128,512]{1,0:T(8,128)(2,1)S(1)}, bf16[128,512]{1,0:T(8,128)(2,1)S(1)}, u32[]{:S(2)}, u32[]{:S(2)}) collective-permute-start(bf16[128,512]{1,0:T(8,128)(2,1)S(1)} %pad_maximum_fusion.3), channel_id=1, source_target_pairs={{0,2},{2,0},{4,6},{6,4},{8,10},{10,8},{12,14},{14,12},{1,3},{3,1},... | collective-permute-start | bytes 393224 | tf_op jit(solution)/shard_map/ppermute | solution.py:18
  35.6 5.0 %collective-permute-start.9 = (bf16[128,512]{1,0:T(8,128)(2,1)S(1)}, bf16[128,512]{1,0:T(8,128)(2,1)S(1)}, u32[]{:S(2)}, u32[]{:S(2)}) collective-permute-start(bf16[128,512]{1,0:T(8,128)(2,1)S(1)} %pad_maximum_fusion.2), channel_id=1, source_target_pairs={{0,4},{2,6},{4,0},{6,2},{8,12},{10,14},{12,8},{14,10},{1,5},{3,7},... | collective-permute-start | bytes 393224 | tf_op jit(solution)/shard_map/ppermute | solution.py:18
  37.1 5.0 %collective-permute-start.4 = (bf16[128,512]{1,0:T(8,128)(2,1)S(1)}, bf16[128,512]{1,0:T(8,128)(2,1)S(1)}, u32[]{:S(2)}, u32[]{:S(2)}) collective-permute-start(bf16[128,512]{1,0:T(8,128)(2,1)S(1)} %pad_maximum_fusion.1), channel_id=1, source_target_pairs={{0,2},{2,0},{4,6},{6,4},{8,10},{10,8},{12,14},{14,12},{1,3},{3,1},... | collective-permute-start | bytes 393224 | tf_op jit(solution)/shard_map/ppermute | solution.py:18
  42.6 1.6 %collective-permute-start.20 = (f32[512,128]{1,0:T(8,128)S(1)}, f32[512,128]{1,0:T(8,128)S(1)}, u32[]{:S(2)}, u32[]{:S(2)}) collective-permute-start(f32[512,128]{1,0:T(8,128)S(1)} %fusion.2.mine_ref), channel_id=1, source_target_pairs={{0,1},{1,0},{2,3},{3,2},{4,5},{5,4},{6,7},{7,6},{8,9},{9,8},{10,11... | collective-permute-start | bytes 786440 | tf_op jit(solution)/shard_map/ppermute | solution.py:18
  44.7 6.6 %collective-permute-start.24 = (f32[72,128]{1,0:T(8,128)S(1)}, f32[72,128]{1,0:T(8,128)S(1)}, u32[]{:S(2)}, u32[]{:S(2)}) collective-permute-start(f32[72,128]{1,0:T(8,128)S(1)} %get-tuple-element.17), channel_id=1, source_target_pairs={{0,10},{1,15},{2,8},{3,13},{4,14},{5,11},{6,12},{7,9},{8,2},{9,7},... | collective-permute-start | bytes 110600 | tf_op jit(solution)/shard_map/ppermute | solution.py:36
  47.0 5.5 %collective-permute-start.23 = (f32[72,128]{1,0:T(8,128)S(1)}, f32[72,128]{1,0:T(8,128)S(1)}, u32[]{:S(2)}, u32[]{:S(2)}) collective-permute-start(f32[72,128]{1,0:T(8,128)S(1)} %get-tuple-element.17), channel_id=1, source_target_pairs={{0,8},{1,13},{2,10},{3,15},{4,12},{5,9},{6,14},{7,11},{8,0},{9,5},... | collective-permute-start | bytes 110600 | tf_op jit(solution)/shard_map/ppermute | solution.py:36
  48.0 4.5 %collective-permute-start.22 = (f32[72,128]{1,0:T(8,128)S(1)}, f32[72,128]{1,0:T(8,128)S(1)}, u32[]{:S(2)}, u32[]{:S(2)}) collective-permute-start(f32[72,128]{1,0:T(8,128)S(1)} %get-tuple-element.17), channel_id=1, source_target_pairs={{0,2},{1,7},{2,0},{3,5},{4,6},{5,3},{6,4},{7,1},{8,10},{9,15},{10,... | collective-permute-start | bytes 110600 | tf_op jit(solution)/shard_map/ppermute | solution.py:36
  49.2 3.3 %collective-permute-start.21 = (f32[72,128]{1,0:T(8,128)S(1)}, f32[72,128]{1,0:T(8,128)S(1)}, u32[]{:S(2)}, u32[]{:S(2)}) collective-permute-start(f32[72,128]{1,0:T(8,128)S(1)} %get-tuple-element.17), channel_id=1, source_target_pairs={{1,5},{3,7},{5,1},{7,3},{9,13},{11,15},{13,9},{15,11},{17,21},{19,... | collective-permute-start | bytes 110600 | tf_op jit(solution)/shard_map/ppermute | solution.py:36
  52.5 2.2 %collective-permute-start.25 = (f32[72,128]{1,0:T(8,128)S(1)}, f32[72,128]{1,0:T(8,128)S(1)}, u32[]{:S(2)}, u32[]{:S(2)}) collective-permute-start(f32[72,128]{1,0:T(8,128)S(1)} %add_add_fusion), channel_id=1, source_target_pairs={{0,1},{1,0},{2,3},{3,2},{4,5},{5,4},{6,7},{7,6},{8,9},{9,8},{10,11... | collective-permute-start | bytes 110600 | tf_op jit(solution)/shard_map/ppermute | solution.py:18
  59.0 6.3 %collective-permute-start.26 = (bf16[2,2,16,1024]{3,2,0,1:T(8,128)(2,1)S(1)}, bf16[2,2,16,1024]{3,2,0,1:T(8,128)(2,1)S(1)}, u32[]{:S(2)}, u32[]{:S(2)}) collective-permute-start(bf16[2,2,16,1024]{3,2,0,1:T(8,128)(2,1)S(1)} %fusion.22), channel_id=1, source_target_pairs={{0,2},{2,0},{4,6},{6,4},{8,10},{10,8},{12,14},{14,12},{1,3},{3,1},... | collective-permute-start | bytes 393224 | tf_op jit(solution)/shard_map/ppermute | solution.py:18
  59.9 7.3 %collective-permute-start.29 = (bf16[2,2,16,1024]{3,2,0,1:T(8,128)(2,1)S(1)}, bf16[2,2,16,1024]{3,2,0,1:T(8,128)(2,1)S(1)}, u32[]{:S(2)}, u32[]{:S(2)}) collective-permute-start(bf16[2,2,16,1024]{3,2,0,1:T(8,128)(2,1)S(1)} %fusion.23), channel_id=1, source_target_pairs={{0,4},{2,6},{4,0},{6,2},{8,12},{10,14},{12,8},{14,10},{1,5},{3,7},... | collective-permute-start | bytes 393224 | tf_op jit(solution)/shard_map/ppermute | solution.py:18
  61.8 6.4 %collective-permute-start.32 = (bf16[2,2,16,1024]{3,2,0,1:T(8,128)(2,1)S(1)}, bf16[2,2,16,1024]{3,2,0,1:T(8,128)(2,1)S(1)}, u32[]{:S(2)}, u32[]{:S(2)}) collective-permute-start(bf16[2,2,16,1024]{3,2,0,1:T(8,128)(2,1)S(1)} %fusion.24), channel_id=1, source_target_pairs={{0,2},{2,0},{4,6},{6,4},{8,10},{10,8},{12,14},{14,12},{1,3},{3,1},... | collective-permute-start | bytes 393224 | tf_op jit(solution)/shard_map/ppermute | solution.py:18
  63.1 6.4 %collective-permute-start.35 = (bf16[2,2,16,1024]{3,2,0,1:T(8,128)(2,1)S(1)}, bf16[2,2,16,1024]{3,2,0,1:T(8,128)(2,1)S(1)}, u32[]{:S(2)}, u32[]{:S(2)}) collective-permute-start(bf16[2,2,16,1024]{3,2,0,1:T(8,128)(2,1)S(1)} %fusion.25), channel_id=1, source_target_pairs={{0,4},{2,6},{4,0},{6,2},{8,12},{10,14},{12,8},{14,10},{1,5},{3,7},... | collective-permute-start | bytes 393224 | tf_op jit(solution)/shard_map/ppermute | solution.py:18
  65.3 5.2 %collective-permute-start.27 = (bf16[2,16,1024]{2,1,0:T(8,128)(2,1)S(1)}, bf16[2,16,1024]{2,1,0:T(8,128)(2,1)S(1)}, u32[]{:S(2)}, u32[]{:S(2)}) collective-permute-start(bf16[2,16,1024]{2,1,0:T(8,128)(2,1)S(1)} %fusion.26), channel_id=1, source_target_pairs={{0,4},{2,6},{4,0},{6,2},{8,12},{10,14},{12,8},{14,10},{1,5},{3,7},... | collective-permute-start | bytes 196616 | tf_op jit(solution)/shard_map/ppermute | solution.py:18
  67.3 5.1 %collective-permute-start.30 = (bf16[2,16,1024]{2,1,0:T(8,128)(2,1)S(1)}, bf16[2,16,1024]{2,1,0:T(8,128)(2,1)S(1)}, u32[]{:S(2)}, u32[]{:S(2)}) collective-permute-start(bf16[2,16,1024]{2,1,0:T(8,128)(2,1)S(1)} %fusion.27), channel_id=1, source_target_pairs={{0,2},{2,0},{4,6},{6,4},{8,10},{10,8},{12,14},{14,12},{1,3},{3,1},... | collective-permute-start | bytes 196616 | tf_op jit(solution)/shard_map/ppermute | solution.py:18
  68.2 5.4 %collective-permute-start.33 = (bf16[2,16,1024]{2,1,0:T(8,128)(2,1)S(1)}, bf16[2,16,1024]{2,1,0:T(8,128)(2,1)S(1)}, u32[]{:S(2)}, u32[]{:S(2)}) collective-permute-start(bf16[2,16,1024]{2,1,0:T(8,128)(2,1)S(1)} %fusion.28), channel_id=1, source_target_pairs={{0,4},{2,6},{4,0},{6,2},{8,12},{10,14},{12,8},{14,10},{1,5},{3,7},... | collective-permute-start | bytes 196616 | tf_op jit(solution)/shard_map/ppermute | solution.py:18
  69.6 5.9 %collective-permute-start.36 = (bf16[2,16,1024]{2,1,0:T(8,128)(2,1)S(1)}, bf16[2,16,1024]{2,1,0:T(8,128)(2,1)S(1)}, u32[]{:S(2)}, u32[]{:S(2)}) collective-permute-start(bf16[2,16,1024]{2,1,0:T(8,128)(2,1)S(1)} %fusion.29), channel_id=1, source_target_pairs={{0,2},{2,0},{4,6},{6,4},{8,10},{10,8},{12,14},{14,12},{1,3},{3,1},... | collective-permute-start | bytes 196616 | tf_op jit(solution)/shard_map/ppermute | solution.py:18
  70.5 6.3 %collective-permute-start.28 = (bf16[16,1024]{1,0:T(8,128)(2,1)S(1)}, bf16[16,1024]{1,0:T(8,128)(2,1)S(1)}, u32[]{:S(2)}, u32[]{:S(2)}) collective-permute-start(bf16[16,1024]{1,0:T(8,128)(2,1)S(1)} %fusion.34), channel_id=1, source_target_pairs={{0,8},{2,10},{4,12},{6,14},{8,0},{10,2},{12,4},{14,6},{1,9},{3,11}... | collective-permute-start | bytes 98312 | tf_op jit(solution)/shard_map/ppermute | solution.py:18
  72.4 5.7 %collective-permute-start.31 = (bf16[16,1024]{1,0:T(8,128)(2,1)S(1)}, bf16[16,1024]{1,0:T(8,128)(2,1)S(1)}, u32[]{:S(2)}, u32[]{:S(2)}) collective-permute-start(bf16[16,1024]{1,0:T(8,128)(2,1)S(1)} %fusion.35), channel_id=1, source_target_pairs={{0,8},{2,10},{4,12},{6,14},{8,0},{10,2},{12,4},{14,6},{1,9},{3,11}... | collective-permute-start | bytes 98312 | tf_op jit(solution)/shard_map/ppermute | solution.py:18
  73.7 5.0 %collective-permute-start.34 = (bf16[16,1024]{1,0:T(8,128)(2,1)S(1)}, bf16[16,1024]{1,0:T(8,128)(2,1)S(1)}, u32[]{:S(2)}, u32[]{:S(2)}) collective-permute-start(bf16[16,1024]{1,0:T(8,128)(2,1)S(1)} %fusion.36), channel_id=1, source_target_pairs={{0,8},{2,10},{4,12},{6,14},{8,0},{10,2},{12,4},{14,6},{1,9},{3,11}... | collective-permute-start | bytes 98312 | tf_op jit(solution)/shard_map/ppermute | solution.py:18
  75.6 5.2 %collective-permute-start.37 = (bf16[16,1024]{1,0:T(8,128)(2,1)S(1)}, bf16[16,1024]{1,0:T(8,128)(2,1)S(1)}, u32[]{:S(2)}, u32[]{:S(2)}) collective-permute-start(bf16[16,1024]{1,0:T(8,128)(2,1)S(1)} %fusion.37), channel_id=1, source_target_pairs={{0,8},{2,10},{4,12},{6,14},{8,0},{10,2},{12,4},{14,6},{1,9},{3,11}... | collective-permute-start | bytes 98312 | tf_op jit(solution)/shard_map/ppermute | solution.py:18

commit v26 on v25

--- a/solution.py
+++ b/solution.py
@@ -9,6 +9,7 @@
 from jax.sharding import PartitionSpec as P
 
 CHUNKS = 4
+LAST_CHUNKS = 2
 TILE = 512
 KERNEL_VMEM = 50 * 2**20
 
@@ -42,20 +43,27 @@
     return value
 
 
-def scatter_sum(value, axis, order):
-    rows, cols = value.shape[0] >> len(order), value.shape[1]
-    total = value.reshape([2] * len(order) + [rows, cols])
-    left = sorted(order, reverse=True)
-    for bit in order:
-        dim = left.index(bit)
-        left.remove(bit)
-        low = lax.index_in_dim(total, 0, dim, keepdims=False)
-        high = lax.index_in_dim(total, 1, dim, keepdims=False)
-        upper = bit_of(axis, bit) == 1
-        send = jnp.where(upper, low, high).astype(jnp.bfloat16)
-        landed = swap(send, axis, 1 << bit)
-        total = jnp.where(upper, high, low) + landed.astype(jnp.float32)
-    return total
+def levels_of(size):
+    levels, stride = [], 1
+    while stride < size:
+        radix = 2 if stride == 1 else min(4, size // stride)
+        levels.append((stride, radix))
+        stride *= radix
+    return levels
+
+
+def scatter_sum(value, axis):
+    size, cols = lax.axis_size(axis), value.shape[1]
+    total = value.reshape(size, value.shape[0] // size, cols)
+    for stride, radix in levels_of(size):
+        digit = lax.rem(lax.div(lax.axis_index(axis), stride), radix)
+        view = total.reshape((total.shape[0] // radix, radix) + total.shape[1:])
+        total = lax.dynamic_index_in_dim(view, digit, 1, keepdims=False)
+        for t in range(1, radix):
+            part = lax.dynamic_index_in_dim(view, jnp.bitwise_xor(digit, t), 1, keepdims=False)
+            landed = swap(part.astype(jnp.bfloat16), axis, t * stride)
+            total = total + landed.astype(jnp.float32)
+    return total[0]
 
 
 def bit_of(axis, bit):
@@ -321,11 +329,8 @@
         )
     other_sketch = swap(partial_sketch, "col", 1)
     packed, sketch = make_gram(partial_sketch, other_sketch, total_cols)
-    basis, *products = make_basis(row_sum(packed), sketch, activations, root_rows, CHUNKS)
-    pieces = [
-        scatter_sum(product, "row", orders[c % 2]) / total_rows
-        for c, product in enumerate(products)
-    ]
+    basis, *products = make_basis(row_sum(packed), sketch, activations, root_rows, LAST_CHUNKS)
+    pieces = [scatter_sum(product, "row") / total_rows for product in products]
     return (basis, jnp.concatenate(pieces, axis=1))
 
 

time: 81.8 us -> 85.2 us (1.042)
  waiting for transfers between devices: 22.3 us -> 31.1 us
  starting transfers between devices: 44.5 us -> 39.5 us
    ppermute x34 -> x30, waiting for transfers between devices: 19.6 us -> 26.5 us  [swap(): return lax.ppermute(value, axis, [(i, i ^ distance) for i in range(size)])]
    ppermute x34 -> x30, starting transfers between devices: 39.4 us -> 34.4 us  [swap(): return lax.ppermute(value, axis, [(i, i ^ distance) for i in range(size)])]
    ppermute x4, waiting for transfers between devices: 2.67 us -> 4.64 us  [row_sum(): terms.append(lax.ppermute(value, ('row', 'col'), pairs))]
  transfers between devices with their start and end apart: 38 -> 34, of which waited for: 19 -> 20; matrix products, arithmetic and copies ran while one was open for 3% -> 3% of each run, Pallas kernels for 2% -> 2%
where the time goes in v26:
time: 85.2 us; the launch traced here: 84.9 us
  starting transfers between devices  39.5 us (46%)
  waiting for transfers between devices  31.1 us (37%)
  Pallas kernels  8.67 us (10%)
  other arithmetic  1.79 us (2%)
  matrix products  1.78 us (2%)
  local copies, waits for them, and re-layouts  1.04 us (1%)
  between operations  1.01 us (1%)
    ppermute x30, starting transfers between devices, swap(): return lax.ppermute(value, axis, [(i, i ^ distance) for i in range(size)])  34.4 us
    ppermute x30, waiting for transfers between devices, swap(): return lax.ppermute(value, axis, [(i, i ^ distance) for i in range(size)])  26.5 us
    ppermute x4, starting transfers between devices, row_sum(): terms.append(lax.ppermute(value, ('row', 'col'), pairs))  5.12 us
    ppermute x4, waiting for transfers between devices, row_sum(): terms.append(lax.ppermute(value, ('row', 'col'), pairs))  4.64 us
    pallas_call x1, Pallas kernels, make_basis(): pl.pallas_call(functools.partial(basis_kernel, root_rows), out_shape=[jax...  4.1 us
    pallas_call x2, Pallas kernels, first_product(): pl.pallas_call(functools.partial(sketch_kernel, begin), out_shape=[jax.Sh...  4.07 us
    dot_general x4, matrix products, per_device(): lax.dot_general(activations[:, span], shared, (((1,), (1,)), ((), ())), p...  1.78 us
  transfers between devices with their start and end apart: 34, of which 20 were waited for; matrix products, arithmetic and copies ran while one was open for 3% of the time, Pallas kernels for 2%

profile of v26, /device:TPU:0, one launch (start us, length us, event | category | flops | bytes accessed | tf_op | source)
XLA Modules:
  0.0 84.9 jit_solution(12507934809318297765)
XLA Ops:
  0.6 0.9 %copy-done = bf16[512,128]{1,0:T(8,128)(2,1)S(1)} copy-done((bf16[512,128]{1,0:T(8,128)(2,1)S(1)}, bf16[512,128]{1,0:T(8,128)(2,1)}, u32[]{:S(2)}) %copy-start) | copy-done | bytes 131096
  1.5 2.1 %first_product.2 = (f32[128,1024]{1,0:T(8,128)S(1)}, f32[128,1024]{1,0:T(8,128)S(1)}) custom-call(bf16[512,128]{1,0:T(8,128)(2,1)S(1)} %copy-done, bf16[512,4096]{1,0:T(8,128)(2,1)} %slab_ref.5), custom_call_target="tpu_custom_call" | custom-call | flops 268435456 | bytes 2097152 | tf_op jit(solution)/shard_map/first_product/pallas_call | solution.py:125
  3.6 3.0 %collective-permute-start = (bf16[128,512]{1,0:T(8,128)(2,1)S(1)}, bf16[128,512]{1,0:T(8,128)(2,1)S(1)}, u32[]{:S(2)}, u32[]{:S(2)}) collective-permute-start(bf16[128,512]{1,0:T(8,128)(2,1)S(1)} %select_convert_fusion.3), channel_id=1, source_target_pairs={{0,2},{2,0},{4,6},{6,4},{8,10},{10,8},{12,14},{14,12},{1,3},{3,1},... | collective-permute-start | bytes 393224 | tf_op jit(solution)/shard_map/ppermute | solution.py:19
  6.7 1.6 %collective-permute-start.5 = (bf16[128,512]{1,0:T(8,128)(2,1)S(1)}, bf16[128,512]{1,0:T(8,128)(2,1)S(1)}, u32[]{:S(2)}, u32[]{:S(2)}) collective-permute-start(bf16[128,512]{1,0:T(8,128)(2,1)S(1)} %select_convert_fusion.2), channel_id=1, source_target_pairs={{0,4},{2,6},{4,0},{6,2},{8,12},{10,14},{12,8},{14,10},{1,5},{3,7},... | collective-permute-start | bytes 393224 | tf_op jit(solution)/shard_map/ppermute | solution.py:19
  8.3 2.0 %first_product.3 = (f32[128,1024]{1,0:T(8,128)S(1)}, f32[128,1024]{1,0:T(8,128)S(1)}) custom-call(bf16[512,128]{1,0:T(8,128)(2,1)S(1)} %copy-done.1, bf16[512,4096]{1,0:T(8,128)(2,1)} %slab_ref.5), custom_call_target="tpu_custom_call" | custom-call | flops 268435456 | bytes 2097152 | tf_op jit(solution)/shard_map/first_product/pallas_call | solution.py:125
  10.4 0.6 collective-permute-start.10
  11.2 2.1 %collective-permute-start.1 = (bf16[128,256]{1,0:T(8,128)(2,1)S(1)}, bf16[128,256]{1,0:T(8,128)(2,1)S(1)}, u32[]{:S(2)}, u32[]{:S(2)}) collective-permute-start(bf16[128,256]{1,0:T(8,128)(2,1)S(1)} %select_convert_fusion.7), channel_id=1, source_target_pairs={{0,4},{2,6},{4,0},{6,2},{8,12},{10,14},{12,8},{14,10},{1,5},{3,7},... | collective-permute-start | bytes 196616 | tf_op jit(solution)/shard_map/ppermute | solution.py:19
  13.3 1.6 %collective-permute-start.6 = (bf16[128,256]{1,0:T(8,128)(2,1)S(1)}, bf16[128,256]{1,0:T(8,128)(2,1)S(1)}, u32[]{:S(2)}, u32[]{:S(2)}) collective-permute-start(bf16[128,256]{1,0:T(8,128)(2,1)S(1)} %select_convert_fusion.6), channel_id=1, source_target_pairs={{0,2},{2,0},{4,6},{6,4},{8,10},{10,8},{12,14},{14,12},{1,3},{3,1},... | collective-permute-start | bytes 196616 | tf_op jit(solution)/shard_map/ppermute | solution.py:19
  14.9 1.2 %collective-permute-done.10 = bf16[128,512]{1,0:T(8,128)(2,1)S(1)} collective-permute-done((bf16[128,512]{1,0:T(8,128)(2,1)S(1)}, bf16[128,512]{1,0:T(8,128)(2,1)S(1)}, u32[]{:S(2)}, u32[]{:S(2)}) %collective-permute-start.10) | collective-permute-done | bytes 131104 | tf_op jit(solution)/shard_map/ppermute | solution.py:19
  16.2 0.5 collective-permute-start.11
  16.8 1.7 %collective-permute-start.16 = (bf16[128,256]{1,0:T(8,128)(2,1)S(1)}, bf16[128,256]{1,0:T(8,128)(2,1)S(1)}, u32[]{:S(2)}, u32[]{:S(2)}) collective-permute-start(bf16[128,256]{1,0:T(8,128)(2,1)S(1)} %select_convert_fusion.4), channel_id=1, source_target_pairs={{0,2},{2,0},{4,6},{6,4},{8,10},{10,8},{12,14},{14,12},{1,3},{3,1},... | collective-permute-start | bytes 196616 | tf_op jit(solution)/shard_map/ppermute | solution.py:19
  18.5 2.7 %collective-permute-start.2 = (bf16[128,256]{1,0:T(8,128)(2,1)S(1)}, bf16[128,256]{1,0:T(8,128)(2,1)S(1)}, u32[]{:S(2)}, u32[]{:S(2)}) collective-permute-start(bf16[128,256]{1,0:T(8,128)(2,1)S(1)} %fusion.24), channel_id=1, source_target_pairs={{0,8},{2,10},{4,12},{6,14},{8,0},{10,2},{12,4},{14,6},{1,9},{3,11}... | collective-permute-start | bytes 196616 | tf_op jit(solution)/shard_map/ppermute | solution.py:19
  21.7 2.7 %collective-permute-start.12 = (bf16[128,256]{1,0:T(8,128)(2,1)S(1)}, bf16[128,256]{1,0:T(8,128)(2,1)S(1)}, u32[]{:S(2)}, u32[]{:S(2)}) collective-permute-start(bf16[128,256]{1,0:T(8,128)(2,1)S(1)} %fusion.26), channel_id=1, source_target_pairs={{0,8},{2,10},{4,12},{6,14},{8,0},{10,2},{12,4},{14,6},{1,9},{3,11}... | collective-permute-start | bytes 196616 | tf_op jit(solution)/shard_map/ppermute | solution.py:19
  24.7 3.0 %collective-permute-done.2 = bf16[128,256]{1,0:T(8,128)(2,1)S(1)} collective-permute-done((bf16[128,256]{1,0:T(8,128)(2,1)S(1)}, bf16[128,256]{1,0:T(8,128)(2,1)S(1)}, u32[]{:S(2)}, u32[]{:S(2)}) %collective-permute-start.2) | collective-permute-done | bytes 65568 | tf_op jit(solution)/shard_map/ppermute | solution.py:19
  27.9 2.0 %collective-permute-done.7 = bf16[128,256]{1,0:T(8,128)(2,1)S(1)} collective-permute-done((bf16[128,256]{1,0:T(8,128)(2,1)S(1)}, bf16[128,256]{1,0:T(8,128)(2,1)S(1)}, u32[]{:S(2)}, u32[]{:S(2)}) %collective-permute-start.7) | collective-permute-done | bytes 65568 | tf_op jit(solution)/shard_map/ppermute | solution.py:19
  30.0 0.5 collective-permute-done.12
  30.7 0.7 collective-permute-done.17
  31.4 1.1 %collective-permute-start.18 = (bf16[128,256]{1,0:T(8,128)(2,1)S(1)}, bf16[128,256]{1,0:T(8,128)(2,1)S(1)}, u32[]{:S(2)}, u32[]{:S(2)}) collective-permute-start(bf16[128,256]{1,0:T(8,128)(2,1)S(1)} %multiply_convert_fusion), channel_id=1, source_target_pairs={{0,2},{2,0},{4,6},{6,4},{8,10},{10,8},{12,14},{14,12},{1,3},{3,1},... | collective-permute-start | bytes 196616 | tf_op jit(solution)/shard_map/ppermute | solution.py:19
  32.7 0.9 %collective-permute-start.4 = (bf16[128,512]{1,0:T(8,128)(2,1)S(1)}, bf16[128,512]{1,0:T(8,128)(2,1)S(1)}, u32[]{:S(2)}, u32[]{:S(2)}) collective-permute-start(bf16[128,512]{1,0:T(8,128)(2,1)S(1)} %pad_maximum_fusion.1), channel_id=1, source_target_pairs={{0,2},{2,0},{4,6},{6,4},{8,10},{10,8},{12,14},{14,12},{1,3},{3,1},... | collective-permute-start | bytes 393224 | tf_op jit(solution)/shard_map/ppermute | solution.py:19
  33.6 1.2 %collective-permute-done.8 = bf16[128,256]{1,0:T(8,128)(2,1)S(1)} collective-permute-done((bf16[128,256]{1,0:T(8,128)(2,1)S(1)}, bf16[128,256]{1,0:T(8,128)(2,1)S(1)}, u32[]{:S(2)}, u32[]{:S(2)}) %collective-permute-start.8) | collective-permute-done | bytes 65568 | tf_op jit(solution)/shard_map/ppermute | solution.py:19
  35.5 1.6 %collective-permute-start.14 = (bf16[128,512]{1,0:T(8,128)(2,1)S(1)}, bf16[128,512]{1,0:T(8,128)(2,1)S(1)}, u32[]{:S(2)}, u32[]{:S(2)}) collective-permute-start(bf16[128,512]{1,0:T(8,128)(2,1)S(1)} %pad_maximum_fusion.3), channel_id=1, source_target_pairs={{0,2},{2,0},{4,6},{6,4},{8,10},{10,8},{12,14},{14,12},{1,3},{3,1},... | collective-permute-start | bytes 393224 | tf_op jit(solution)/shard_map/ppermute | solution.py:19
  37.2 0.7 collective-permute-start.19
  37.8 1.9 %collective-permute-done.9 = bf16[128,512]{1,0:T(8,128)(2,1)S(1)} collective-permute-done((bf16[128,512]{1,0:T(8,128)(2,1)S(1)}, bf16[128,512]{1,0:T(8,128)(2,1)S(1)}, u32[]{:S(2)}, u32[]{:S(2)}) %collective-permute-start.9) | collective-permute-done | bytes 131104 | tf_op jit(solution)/shard_map/ppermute | solution.py:19
  41.1 1.1 %collective-permute-done.19 = bf16[128,512]{1,0:T(8,128)(2,1)S(1)} collective-permute-done((bf16[128,512]{1,0:T(8,128)(2,1)S(1)}, bf16[128,512]{1,0:T(8,128)(2,1)S(1)}, u32[]{:S(2)}, u32[]{:S(2)}) %collective-permute-start.19) | collective-permute-done | bytes 131104 | tf_op jit(solution)/shard_map/ppermute | solution.py:19
  42.8 0.5 fusion.2.mine_ref
  43.3 1.5 %collective-permute-done.20.other_ref = f32[512,128]{1,0:T(8,128)S(1)} collective-permute-done((f32[512,128]{1,0:T(8,128)S(1)}, f32[512,128]{1,0:T(8,128)S(1)}, u32[]{:S(2)}, u32[]{:S(2)}) %collective-permute-start.20) | collective-permute-done | bytes 262176 | tf_op jit(solution)/shard_map/ppermute | solution.py:19
  44.8 0.5 make_gram.1
  45.3 0.7 collective-permute-start.21
  46.0 0.6 collective-permute-start.22
  46.6 1.7 %collective-permute-start.23 = (f32[72,128]{1,0:T(8,128)S(1)}, f32[72,128]{1,0:T(8,128)S(1)}, u32[]{:S(2)}, u32[]{:S(2)}) collective-permute-start(f32[72,128]{1,0:T(8,128)S(1)} %get-tuple-element.15), channel_id=1, source_target_pairs={{0,8},{1,13},{2,10},{3,15},{4,12},{5,9},{6,14},{7,11},{8,0},{9,5},... | collective-permute-start | bytes 110600 | tf_op jit(solution)/shard_map/ppermute | solution.py:37
  48.3 2.2 %collective-permute-start.24 = (f32[72,128]{1,0:T(8,128)S(1)}, f32[72,128]{1,0:T(8,128)S(1)}, u32[]{:S(2)}, u32[]{:S(2)}) collective-permute-start(f32[72,128]{1,0:T(8,128)S(1)} %get-tuple-element.15), channel_id=1, source_target_pairs={{0,10},{1,15},{2,8},{3,13},{4,14},{5,11},{6,12},{7,9},{8,2},{9,7},... | collective-permute-start | bytes 110600 | tf_op jit(solution)/shard_map/ppermute | solution.py:37
  50.5 1.0 %collective-permute-done.23 = f32[72,128]{1,0:T(8,128)S(1)} collective-permute-done((f32[72,128]{1,0:T(8,128)S(1)}, f32[72,128]{1,0:T(8,128)S(1)}, u32[]{:S(2)}, u32[]{:S(2)}) %collective-permute-start.23) | collective-permute-done | bytes 36896 | tf_op jit(solution)/shard_map/ppermute | solution.py:37
  51.5 3.7 %collective-permute-done.24 = f32[72,128]{1,0:T(8,128)S(1)} collective-permute-done((f32[72,128]{1,0:T(8,128)S(1)}, f32[72,128]{1,0:T(8,128)S(1)}, u32[]{:S(2)}, u32[]{:S(2)}) %collective-permute-start.24) | collective-permute-done | bytes 36896 | tf_op jit(solution)/shard_map/ppermute | solution.py:37
  55.1 1.2 %collective-permute-start.25 = (f32[72,128]{1,0:T(8,128)S(1)}, f32[72,128]{1,0:T(8,128)S(1)}, u32[]{:S(2)}, u32[]{:S(2)}) collective-permute-start(f32[72,128]{1,0:T(8,128)S(1)} %add_add_fusion), channel_id=1, source_target_pairs={{0,1},{1,0},{2,3},{3,2},{4,5},{5,4},{6,7},{7,6},{8,9},{9,8},{10,11... | collective-permute-start | bytes 110600 | tf_op jit(solution)/shard_map/ppermute | solution.py:19
  56.3 0.9 %collective-permute-done.25 = f32[72,128]{1,0:T(8,128)S(1)} collective-permute-done((f32[72,128]{1,0:T(8,128)S(1)}, f32[72,128]{1,0:T(8,128)S(1)}, u32[]{:S(2)}, u32[]{:S(2)}) %collective-permute-start.25) | collective-permute-done | bytes 36896 | tf_op jit(solution)/shard_map/ppermute | solution.py:19
  57.2 4.1 %make_basis.1 = (f32[512,128]{1,0:T(8,128)}, f32[128,2048]{1,0:T(8,128)S(1)}, f32[128,2048]{1,0:T(8,128)S(1)}) custom-call(f32[72,128]{1,0:T(8,128)S(1)} %add.130.gram_ref, f32[128,512]{1,0:T(8,128)S(1)} %get-tuple-element.16.sketch_ref, bf16[512,4096]{1,0:T(8,128)(2,1)} %slab_ref.5), custom_call_target="tpu_custom_call" | custom-call | tf_op jit(solution)/shard_map/make_basis/pallas_call | solution.py:287
  61.3 1.1 %collective-permute-start.26 = (bf16[4,16,2048]{2,1,0:T(8,128)(2,1)S(1)}, bf16[4,16,2048]{2,1,0:T(8,128)(2,1)S(1)}, u32[]{:S(2)}, u32[]{:S(2)}) collective-permute-start(bf16[4,16,2048]{2,1,0:T(8,128)(2,1)S(1)} %fusion.10), channel_id=1, source_target_pairs={{0,2},{2,0},{4,6},{6,4},{8,10},{10,8},{12,14},{14,12},{1,3},{3,1},... | collective-permute-start | bytes 786440 | tf_op jit(solution)/shard_map/ppermute | solution.py:19
  62.4 1.1 %collective-permute-start.30 = (bf16[4,16,2048]{2,1,0:T(8,128)(2,1)S(1)}, bf16[4,16,2048]{2,1,0:T(8,128)(2,1)S(1)}, u32[]{:S(2)}, u32[]{:S(2)}) collective-permute-start(bf16[4,16,2048]{2,1,0:T(8,128)(2,1)S(1)} %fusion.11), channel_id=1, source_target_pairs={{0,2},{2,0},{4,6},{6,4},{8,10},{10,8},{12,14},{14,12},{1,3},{3,1},... | collective-permute-start | bytes 786440 | tf_op jit(solution)/shard_map/ppermute | solution.py:19
  63.5 7.0 %collective-permute-done.26 = bf16[4,16,2048]{2,1,0:T(8,128)(2,1)S(1)} collective-permute-done((bf16[4,16,2048]{2,1,0:T(8,128)(2,1)S(1)}, bf16[4,16,2048]{2,1,0:T(8,128)(2,1)S(1)}, u32[]{:S(2)}, u32[]{:S(2)}) %collective-permute-start.26) | collective-permute-done | bytes 262176 | tf_op jit(solution)/shard_map/ppermute | solution.py:19
  70.7 2.3 %collective-permute-start.28 = (bf16[1,16,2048]{2,1,0:T(8,128)(2,1)S(1)}, bf16[1,16,2048]{2,1,0:T(8,128)(2,1)S(1)}, u32[]{:S(2)}, u32[]{:S(2)}) collective-permute-start(bf16[1,16,2048]{2,1,0:T(8,128)(2,1)S(1)} %get-tuple-element.22), channel_id=1, source_target_pairs={{0,8},{2,10},{4,12},{6,14},{8,0},{10,2},{12,4},{14,6},{1,9},{3,11}... | collective-permute-start | bytes 196616 | tf_op jit(solution)/shard_map/ppermute | solution.py:19
  72.9 2.1 %collective-permute-start.29 = (bf16[1,16,2048]{2,1,0:T(8,128)(2,1)S(1)}, bf16[1,16,2048]{2,1,0:T(8,128)(2,1)S(1)}, u32[]{:S(2)}, u32[]{:S(2)}) collective-permute-start(bf16[1,16,2048]{2,1,0:T(8,128)(2,1)S(1)} %get-tuple-element.21), channel_id=1, source_target_pairs={{0,12},{2,14},{4,8},{6,10},{8,4},{10,6},{12,0},{14,2},{1,13},{3,15... | collective-permute-start | bytes 196616 | tf_op jit(solution)/shard_map/ppermute | solution.py:19
  75.1 0.5 collective-permute-done.30
  75.7 2.3 %collective-permute-start.32 = (bf16[1,16,2048]{2,1,0:T(8,128)(2,1)S(1)}, bf16[1,16,2048]{2,1,0:T(8,128)(2,1)S(1)}, u32[]{:S(2)}, u32[]{:S(2)}) collective-permute-start(bf16[1,16,2048]{2,1,0:T(8,128)(2,1)S(1)} %get-tuple-element.25), channel_id=1, source_target_pairs={{0,8},{2,10},{4,12},{6,14},{8,0},{10,2},{12,4},{14,6},{1,9},{3,11}... | collective-permute-start | bytes 196616 | tf_op jit(solution)/shard_map/ppermute | solution.py:19
  78.0 2.1 %collective-permute-start.33 = (bf16[1,16,2048]{2,1,0:T(8,128)(2,1)S(1)}, bf16[1,16,2048]{2,1,0:T(8,128)(2,1)S(1)}, u32[]{:S(2)}, u32[]{:S(2)}) collective-permute-start(bf16[1,16,2048]{2,1,0:T(8,128)(2,1)S(1)} %get-tuple-element.24), channel_id=1, source_target_pairs={{0,12},{2,14},{4,8},{6,10},{8,4},{10,6},{12,0},{14,2},{1,13},{3,15... | collective-permute-start | bytes 196616 | tf_op jit(solution)/shard_map/ppermute | solution.py:19
  80.2 0.5 collective-permute-done.31
  80.7 2.8 %collective-permute-done.32 = bf16[1,16,2048]{2,1,0:T(8,128)(2,1)S(1)} collective-permute-done((bf16[1,16,2048]{2,1,0:T(8,128)(2,1)S(1)}, bf16[1,16,2048]{2,1,0:T(8,128)(2,1)S(1)}, u32[]{:S(2)}, u32[]{:S(2)}) %collective-permute-start.32) | collective-permute-done | bytes 65568 | tf_op jit(solution)/shard_map/ppermute | solution.py:19
  83.5 0.7 collective-permute-done.33
  84.2 0.7 pad_maximum_fusion
  (77 shorter events, 5.2 us)
Async XLA Ops:
  0.6 0.9 %copy-start = (bf16[512,128]{1,0:T(8,128)(2,1)S(1)}, bf16[512,128]{1,0:T(8,128)(2,1)}, u32[]{:S(2)}) copy-start(bf16[512,128]{1,0:T(8,128)(2,1)} %start_ref.3) | copy-start | bytes 393220
  1.5 6.8 %copy-start.1 = (bf16[512,128]{1,0:T(8,128)(2,1)S(1)}, bf16[512,128]{1,0:T(8,128)(2,1)}, u32[]{:S(2)}) copy-start(bf16[512,128]{1,0:T(8,128)(2,1)} %start_ref.3) | copy-start | bytes 393220
  3.6 7.5 %collective-permute-start = (bf16[128,512]{1,0:T(8,128)(2,1)S(1)}, bf16[128,512]{1,0:T(8,128)(2,1)S(1)}, u32[]{:S(2)}, u32[]{:S(2)}) collective-permute-start(bf16[128,512]{1,0:T(8,128)(2,1)S(1)} %select_convert_fusion.3), channel_id=1, source_target_pairs={{0,2},{2,0},{4,6},{6,4},{8,10},{10,8},{12,14},{14,12},{1,3},{3,1},... | collective-permute-start | bytes 393224 | tf_op jit(solution)/shard_map/ppermute | solution.py:19
  6.7 6.6 %collective-permute-start.5 = (bf16[128,512]{1,0:T(8,128)(2,1)S(1)}, bf16[128,512]{1,0:T(8,128)(2,1)S(1)}, u32[]{:S(2)}, u32[]{:S(2)}) collective-permute-start(bf16[128,512]{1,0:T(8,128)(2,1)S(1)} %select_convert_fusion.2), channel_id=1, source_target_pairs={{0,4},{2,6},{4,0},{6,2},{8,12},{10,14},{12,8},{14,10},{1,5},{3,7},... | collective-permute-start | bytes 393224 | tf_op jit(solution)/shard_map/ppermute | solution.py:19
  10.4 5.7 %collective-permute-start.10 = (bf16[128,512]{1,0:T(8,128)(2,1)S(1)}, bf16[128,512]{1,0:T(8,128)(2,1)S(1)}, u32[]{:S(2)}, u32[]{:S(2)}) collective-permute-start(bf16[128,512]{1,0:T(8,128)(2,1)S(1)} %select_convert_fusion.1), channel_id=1, source_target_pairs={{0,2},{2,0},{4,6},{6,4},{8,10},{10,8},{12,14},{14,12},{1,3},{3,1},... | collective-permute-start | bytes 393224 | tf_op jit(solution)/shard_map/ppermute | solution.py:19
  11.0 5.7 %collective-permute-start.15 = (bf16[128,512]{1,0:T(8,128)(2,1)S(1)}, bf16[128,512]{1,0:T(8,128)(2,1)S(1)}, u32[]{:S(2)}, u32[]{:S(2)}) collective-permute-start(bf16[128,512]{1,0:T(8,128)(2,1)S(1)} %select_convert_fusion), channel_id=1, source_target_pairs={{0,4},{2,6},{4,0},{6,2},{8,12},{10,14},{12,8},{14,10},{1,5},{3,7},... | collective-permute-start | bytes 393224 | tf_op jit(solution)/shard_map/ppermute | solution.py:19
  11.2 7.3 %collective-permute-start.1 = (bf16[128,256]{1,0:T(8,128)(2,1)S(1)}, bf16[128,256]{1,0:T(8,128)(2,1)S(1)}, u32[]{:S(2)}, u32[]{:S(2)}) collective-permute-start(bf16[128,256]{1,0:T(8,128)(2,1)S(1)} %select_convert_fusion.7), channel_id=1, source_target_pairs={{0,4},{2,6},{4,0},{6,2},{8,12},{10,14},{12,8},{14,10},{1,5},{3,7},... | collective-permute-start | bytes 196616 | tf_op jit(solution)/shard_map/ppermute | solution.py:19
  13.3 26.5 %copy-start.2 = (bf16[512,4096]{1,0:T(8,128)(2,1)S(1)}, bf16[512,4096]{1,0:T(8,128)(2,1)}, u32[]{:S(2)}) copy-start(bf16[512,4096]{1,0:T(8,128)(2,1)} %slab_ref.5) | copy-start | bytes 12582916
  13.3 7.9 %collective-permute-start.6 = (bf16[128,256]{1,0:T(8,128)(2,1)S(1)}, bf16[128,256]{1,0:T(8,128)(2,1)S(1)}, u32[]{:S(2)}, u32[]{:S(2)}) collective-permute-start(bf16[128,256]{1,0:T(8,128)(2,1)S(1)} %select_convert_fusion.6), channel_id=1, source_target_pairs={{0,2},{2,0},{4,6},{6,4},{8,10},{10,8},{12,14},{14,12},{1,3},{3,1},... | collective-permute-start | bytes 196616 | tf_op jit(solution)/shard_map/ppermute | solution.py:19
  16.2 5.4 %collective-permute-start.11 = (bf16[128,256]{1,0:T(8,128)(2,1)S(1)}, bf16[128,256]{1,0:T(8,128)(2,1)S(1)}, u32[]{:S(2)}, u32[]{:S(2)}) collective-permute-start(bf16[128,256]{1,0:T(8,128)(2,1)S(1)} %select_convert_fusion.5), channel_id=1, source_target_pairs={{0,4},{2,6},{4,0},{6,2},{8,12},{10,14},{12,8},{14,10},{1,5},{3,7},... | collective-permute-start | bytes 196616 | tf_op jit(solution)/shard_map/ppermute | solution.py:19
  16.8 7.5 %collective-permute-start.16 = (bf16[128,256]{1,0:T(8,128)(2,1)S(1)}, bf16[128,256]{1,0:T(8,128)(2,1)S(1)}, u32[]{:S(2)}, u32[]{:S(2)}) collective-permute-start(bf16[128,256]{1,0:T(8,128)(2,1)S(1)} %select_convert_fusion.4), channel_id=1, source_target_pairs={{0,2},{2,0},{4,6},{6,4},{8,10},{10,8},{12,14},{14,12},{1,3},{3,1},... | collective-permute-start | bytes 196616 | tf_op jit(solution)/shard_map/ppermute | solution.py:19
  18.5 9.2 %collective-permute-start.2 = (bf16[128,256]{1,0:T(8,128)(2,1)S(1)}, bf16[128,256]{1,0:T(8,128)(2,1)S(1)}, u32[]{:S(2)}, u32[]{:S(2)}) collective-permute-start(bf16[128,256]{1,0:T(8,128)(2,1)S(1)} %fusion.24), channel_id=1, source_target_pairs={{0,8},{2,10},{4,12},{6,14},{8,0},{10,2},{12,4},{14,6},{1,9},{3,11}... | collective-permute-start | bytes 196616 | tf_op jit(solution)/shard_map/ppermute | solution.py:19
  21.2 8.6 %collective-permute-start.7 = (bf16[128,256]{1,0:T(8,128)(2,1)S(1)}, bf16[128,256]{1,0:T(8,128)(2,1)S(1)}, u32[]{:S(2)}, u32[]{:S(2)}) collective-permute-start(bf16[128,256]{1,0:T(8,128)(2,1)S(1)} %fusion.25), channel_id=1, source_target_pairs={{0,8},{2,10},{4,12},{6,14},{8,0},{10,2},{12,4},{14,6},{1,9},{3,11}... | collective-permute-start | bytes 196616 | tf_op jit(solution)/shard_map/ppermute | solution.py:19
  21.7 8.9 %collective-permute-start.12 = (bf16[128,256]{1,0:T(8,128)(2,1)S(1)}, bf16[128,256]{1,0:T(8,128)(2,1)S(1)}, u32[]{:S(2)}, u32[]{:S(2)}) collective-permute-start(bf16[128,256]{1,0:T(8,128)(2,1)S(1)} %fusion.26), channel_id=1, source_target_pairs={{0,8},{2,10},{4,12},{6,14},{8,0},{10,2},{12,4},{14,6},{1,9},{3,11}... | collective-permute-start | bytes 196616 | tf_op jit(solution)/shard_map/ppermute | solution.py:19
  24.3 7.0 %collective-permute-start.17 = (bf16[128,256]{1,0:T(8,128)(2,1)S(1)}, bf16[128,256]{1,0:T(8,128)(2,1)S(1)}, u32[]{:S(2)}, u32[]{:S(2)}) collective-permute-start(bf16[128,256]{1,0:T(8,128)(2,1)S(1)} %fusion.27), channel_id=1, source_target_pairs={{0,8},{2,10},{4,12},{6,14},{8,0},{10,2},{12,4},{14,6},{1,9},{3,11}... | collective-permute-start | bytes 196616 | tf_op jit(solution)/shard_map/ppermute | solution.py:19
  27.8 4.9 %collective-permute-start.3 = (bf16[128,256]{1,0:T(8,128)(2,1)S(1)}, bf16[128,256]{1,0:T(8,128)(2,1)S(1)}, u32[]{:S(2)}, u32[]{:S(2)}) collective-permute-start(bf16[128,256]{1,0:T(8,128)(2,1)S(1)} %multiply_convert_fusion.3), channel_id=1, source_target_pairs={{0,4},{2,6},{4,0},{6,2},{8,12},{10,14},{12,8},{14,10},{1,5},{3,7},... | collective-permute-start | bytes 196616 | tf_op jit(solution)/shard_map/ppermute | solution.py:19
  29.9 4.8 %collective-permute-start.8 = (bf16[128,256]{1,0:T(8,128)(2,1)S(1)}, bf16[128,256]{1,0:T(8,128)(2,1)S(1)}, u32[]{:S(2)}, u32[]{:S(2)}) collective-permute-start(bf16[128,256]{1,0:T(8,128)(2,1)S(1)} %multiply_convert_fusion.2), channel_id=1, source_target_pairs={{0,2},{2,0},{4,6},{6,4},{8,10},{10,8},{12,14},{14,12},{1,3},{3,1},... | collective-permute-start | bytes 196616 | tf_op jit(solution)/shard_map/ppermute | solution.py:19
  30.6 4.9 %collective-permute-start.13 = (bf16[128,256]{1,0:T(8,128)(2,1)S(1)}, bf16[128,256]{1,0:T(8,128)(2,1)S(1)}, u32[]{:S(2)}, u32[]{:S(2)}) collective-permute-start(bf16[128,256]{1,0:T(8,128)(2,1)S(1)} %multiply_convert_fusion.1), channel_id=1, source_target_pairs={{0,4},{2,6},{4,0},{6,2},{8,12},{10,14},{12,8},{14,10},{1,5},{3,7},... | collective-permute-start | bytes 196616 | tf_op jit(solution)/shard_map/ppermute | solution.py:19
  31.4 5.8 %collective-permute-start.18 = (bf16[128,256]{1,0:T(8,128)(2,1)S(1)}, bf16[128,256]{1,0:T(8,128)(2,1)S(1)}, u32[]{:S(2)}, u32[]{:S(2)}) collective-permute-start(bf16[128,256]{1,0:T(8,128)(2,1)S(1)} %multiply_convert_fusion), channel_id=1, source_target_pairs={{0,2},{2,0},{4,6},{6,4},{8,10},{10,8},{12,14},{14,12},{1,3},{3,1},... | collective-permute-start | bytes 196616 | tf_op jit(solution)/shard_map/ppermute | solution.py:19
  32.7 10.0 %collective-permute-start.4 = (bf16[128,512]{1,0:T(8,128)(2,1)S(1)}, bf16[128,512]{1,0:T(8,128)(2,1)S(1)}, u32[]{:S(2)}, u32[]{:S(2)}) collective-permute-start(bf16[128,512]{1,0:T(8,128)(2,1)S(1)} %pad_maximum_fusion.1), channel_id=1, source_target_pairs={{0,2},{2,0},{4,6},{6,4},{8,10},{10,8},{12,14},{14,12},{1,3},{3,1},... | collective-permute-start | bytes 393224 | tf_op jit(solution)/shard_map/ppermute | solution.py:19
  34.7 5.0 %collective-permute-start.9 = (bf16[128,512]{1,0:T(8,128)(2,1)S(1)}, bf16[128,512]{1,0:T(8,128)(2,1)S(1)}, u32[]{:S(2)}, u32[]{:S(2)}) collective-permute-start(bf16[128,512]{1,0:T(8,128)(2,1)S(1)} %pad_maximum_fusion.2), channel_id=1, source_target_pairs={{0,4},{2,6},{4,0},{6,2},{8,12},{10,14},{12,8},{14,10},{1,5},{3,7},... | collective-permute-start | bytes 393224 | tf_op jit(solution)/shard_map/ppermute | solution.py:19
  35.5 5.0 %collective-permute-start.14 = (bf16[128,512]{1,0:T(8,128)(2,1)S(1)}, bf16[128,512]{1,0:T(8,128)(2,1)S(1)}, u32[]{:S(2)}, u32[]{:S(2)}) collective-permute-start(bf16[128,512]{1,0:T(8,128)(2,1)S(1)} %pad_maximum_fusion.3), channel_id=1, source_target_pairs={{0,2},{2,0},{4,6},{6,4},{8,10},{10,8},{12,14},{14,12},{1,3},{3,1},... | collective-permute-start | bytes 393224 | tf_op jit(solution)/shard_map/ppermute | solution.py:19
  37.2 5.0 %collective-permute-start.19 = (bf16[128,512]{1,0:T(8,128)(2,1)S(1)}, bf16[128,512]{1,0:T(8,128)(2,1)S(1)}, u32[]{:S(2)}, u32[]{:S(2)}) collective-permute-start(bf16[128,512]{1,0:T(8,128)(2,1)S(1)} %pad_maximum_fusion.4), channel_id=1, source_target_pairs={{0,4},{2,6},{4,0},{6,2},{8,12},{10,14},{12,8},{14,10},{1,5},{3,7},... | collective-permute-start | bytes 393224 | tf_op jit(solution)/shard_map/ppermute | solution.py:19
  43.2 1.6 %collective-permute-start.20 = (f32[512,128]{1,0:T(8,128)S(1)}, f32[512,128]{1,0:T(8,128)S(1)}, u32[]{:S(2)}, u32[]{:S(2)}) collective-permute-start(f32[512,128]{1,0:T(8,128)S(1)} %fusion.2.mine_ref), channel_id=1, source_target_pairs={{0,1},{1,0},{2,3},{3,2},{4,5},{5,4},{6,7},{7,6},{8,9},{9,8},{10,11... | collective-permute-start | bytes 786440 | tf_op jit(solution)/shard_map/ppermute | solution.py:19
  45.3 5.1 %collective-permute-start.21 = (f32[72,128]{1,0:T(8,128)S(1)}, f32[72,128]{1,0:T(8,128)S(1)}, u32[]{:S(2)}, u32[]{:S(2)}) collective-permute-start(f32[72,128]{1,0:T(8,128)S(1)} %get-tuple-element.15), channel_id=1, source_target_pairs={{1,5},{3,7},{5,1},{7,3},{9,13},{11,15},{13,9},{15,11},{17,21},{19,... | collective-permute-start | bytes 110600 | tf_op jit(solution)/shard_map/ppermute | solution.py:37
  46.0 4.5 %collective-permute-start.22 = (f32[72,128]{1,0:T(8,128)S(1)}, f32[72,128]{1,0:T(8,128)S(1)}, u32[]{:S(2)}, u32[]{:S(2)}) collective-permute-start(f32[72,128]{1,0:T(8,128)S(1)} %get-tuple-element.15), channel_id=1, source_target_pairs={{0,2},{1,7},{2,0},{3,5},{4,6},{5,3},{6,4},{7,1},{8,10},{9,15},{10,... | collective-permute-start | bytes 110600 | tf_op jit(solution)/shard_map/ppermute | solution.py:37
  46.6 4.9 %collective-permute-start.23 = (f32[72,128]{1,0:T(8,128)S(1)}, f32[72,128]{1,0:T(8,128)S(1)}, u32[]{:S(2)}, u32[]{:S(2)}) collective-permute-start(f32[72,128]{1,0:T(8,128)S(1)} %get-tuple-element.15), channel_id=1, source_target_pairs={{0,8},{1,13},{2,10},{3,15},{4,12},{5,9},{6,14},{7,11},{8,0},{9,5},... | collective-permute-start | bytes 110600 | tf_op jit(solution)/shard_map/ppermute | solution.py:37
  48.3 6.8 %collective-permute-start.24 = (f32[72,128]{1,0:T(8,128)S(1)}, f32[72,128]{1,0:T(8,128)S(1)}, u32[]{:S(2)}, u32[]{:S(2)}) collective-permute-start(f32[72,128]{1,0:T(8,128)S(1)} %get-tuple-element.15), channel_id=1, source_target_pairs={{0,10},{1,15},{2,8},{3,13},{4,14},{5,11},{6,12},{7,9},{8,2},{9,7},... | collective-permute-start | bytes 110600 | tf_op jit(solution)/shard_map/ppermute | solution.py:37
  55.1 2.0 %collective-permute-start.25 = (f32[72,128]{1,0:T(8,128)S(1)}, f32[72,128]{1,0:T(8,128)S(1)}, u32[]{:S(2)}, u32[]{:S(2)}) collective-permute-start(f32[72,128]{1,0:T(8,128)S(1)} %add_add_fusion), channel_id=1, source_target_pairs={{0,1},{1,0},{2,3},{3,2},{4,5},{5,4},{6,7},{7,6},{8,9},{9,8},{10,11... | collective-permute-start | bytes 110600 | tf_op jit(solution)/shard_map/ppermute | solution.py:19
  61.3 9.2 %collective-permute-start.26 = (bf16[4,16,2048]{2,1,0:T(8,128)(2,1)S(1)}, bf16[4,16,2048]{2,1,0:T(8,128)(2,1)S(1)}, u32[]{:S(2)}, u32[]{:S(2)}) collective-permute-start(bf16[4,16,2048]{2,1,0:T(8,128)(2,1)S(1)} %fusion.10), channel_id=1, source_target_pairs={{0,2},{2,0},{4,6},{6,4},{8,10},{10,8},{12,14},{14,12},{1,3},{3,1},... | collective-permute-start | bytes 786440 | tf_op jit(solution)/shard_map/ppermute | solution.py:19
  62.4 13.1 %collective-permute-start.30 = (bf16[4,16,2048]{2,1,0:T(8,128)(2,1)S(1)}, bf16[4,16,2048]{2,1,0:T(8,128)(2,1)S(1)}, u32[]{:S(2)}, u32[]{:S(2)}) collective-permute-start(bf16[4,16,2048]{2,1,0:T(8,128)(2,1)S(1)} %fusion.11), channel_id=1, source_target_pairs={{0,2},{2,0},{4,6},{6,4},{8,10},{10,8},{12,14},{14,12},{1,3},{3,1},... | collective-permute-start | bytes 786440 | tf_op jit(solution)/shard_map/ppermute | solution.py:19
  70.6 7.4 %collective-permute-start.27 = (bf16[1,16,2048]{2,1,0:T(8,128)(2,1)S(1)}, bf16[1,16,2048]{2,1,0:T(8,128)(2,1)S(1)}, u32[]{:S(2)}, u32[]{:S(2)}) collective-permute-start(bf16[1,16,2048]{2,1,0:T(8,128)(2,1)S(1)} %get-tuple-element.20), channel_id=1, source_target_pairs={{0,4},{2,6},{4,0},{6,2},{8,12},{10,14},{12,8},{14,10},{1,5},{3,7},... | collective-permute-start | bytes 196616 | tf_op jit(solution)/shard_map/ppermute | solution.py:19
  70.7 9.4 %collective-permute-start.28 = (bf16[1,16,2048]{2,1,0:T(8,128)(2,1)S(1)}, bf16[1,16,2048]{2,1,0:T(8,128)(2,1)S(1)}, u32[]{:S(2)}, u32[]{:S(2)}) collective-permute-start(bf16[1,16,2048]{2,1,0:T(8,128)(2,1)S(1)} %get-tuple-element.22), channel_id=1, source_target_pairs={{0,8},{2,10},{4,12},{6,14},{8,0},{10,2},{12,4},{14,6},{1,9},{3,11}... | collective-permute-start | bytes 196616 | tf_op jit(solution)/shard_map/ppermute | solution.py:19
  72.9 7.2 %collective-permute-start.29 = (bf16[1,16,2048]{2,1,0:T(8,128)(2,1)S(1)}, bf16[1,16,2048]{2,1,0:T(8,128)(2,1)S(1)}, u32[]{:S(2)}, u32[]{:S(2)}) collective-permute-start(bf16[1,16,2048]{2,1,0:T(8,128)(2,1)S(1)} %get-tuple-element.21), channel_id=1, source_target_pairs={{0,12},{2,14},{4,8},{6,10},{8,4},{10,6},{12,0},{14,2},{1,13},{3,15... | collective-permute-start | bytes 196616 | tf_op jit(solution)/shard_map/ppermute | solution.py:19
  75.7 5.0 %collective-permute-start.31 = (bf16[1,16,2048]{2,1,0:T(8,128)(2,1)S(1)}, bf16[1,16,2048]{2,1,0:T(8,128)(2,1)S(1)}, u32[]{:S(2)}, u32[]{:S(2)}) collective-permute-start(bf16[1,16,2048]{2,1,0:T(8,128)(2,1)S(1)} %get-tuple-element.23), channel_id=1, source_target_pairs={{0,4},{2,6},{4,0},{6,2},{8,12},{10,14},{12,8},{14,10},{1,5},{3,7},... | collective-permute-start | bytes 196616 | tf_op jit(solution)/shard_map/ppermute | solution.py:19
  75.7 7.7 %collective-permute-start.32 = (bf16[1,16,2048]{2,1,0:T(8,128)(2,1)S(1)}, bf16[1,16,2048]{2,1,0:T(8,128)(2,1)S(1)}, u32[]{:S(2)}, u32[]{:S(2)}) collective-permute-start(bf16[1,16,2048]{2,1,0:T(8,128)(2,1)S(1)} %get-tuple-element.25), channel_id=1, source_target_pairs={{0,8},{2,10},{4,12},{6,14},{8,0},{10,2},{12,4},{14,6},{1,9},{3,11}... | collective-permute-start | bytes 196616 | tf_op jit(solution)/shard_map/ppermute | solution.py:19
  78.0 6.2 %collective-permute-start.33 = (bf16[1,16,2048]{2,1,0:T(8,128)(2,1)S(1)}, bf16[1,16,2048]{2,1,0:T(8,128)(2,1)S(1)}, u32[]{:S(2)}, u32[]{:S(2)}) collective-permute-start(bf16[1,16,2048]{2,1,0:T(8,128)(2,1)S(1)} %get-tuple-element.24), channel_id=1, source_target_pairs={{0,12},{2,14},{4,8},{6,10},{8,4},{10,6},{12,0},{14,2},{1,13},{3,15... | collective-permute-start | bytes 196616 | tf_op jit(solution)/shard_map/ppermute | solution.py:19

commit v27 on v25

--- a/solution.py
+++ b/solution.py
@@ -9,6 +9,7 @@
 from jax.sharding import PartitionSpec as P
 
 CHUNKS = 4
+LINK_TYPES = (jnp.bfloat16, jnp.float32, jnp.bfloat16)
 TILE = 512
 KERNEL_VMEM = 50 * 2**20
 
@@ -24,21 +25,30 @@
     first = lax.axis_index("col") == 0
     stride = 1
     while stride < rows:
-        radix = min(8, rows // stride)
-        split = min(2, radix // 2)
+        if rows // stride < 8:
+            value = value + swap(value, "row", stride)
+            stride *= 2
+            continue
         terms = []
-        for near in [digit for digit in range(radix) if not digit & split]:
-            pairs = []
-            for row in range(rows):
-                for core, digit in ((0, near), (1, near | split)):
-                    if digit:
-                        pairs.append((row * cores + core, (row ^ digit * stride) * cores + core))
+        for near in range(2):
+            pairs = [
+                (row * 2 + core, (row ^ (near + 2 * core) * stride) * 2 + core)
+                for row in range(rows)
+                for core in range(2)
+                if near + core
+            ]
             terms.append(lax.ppermute(value, ("row", "col"), pairs))
-        terms[0] = jnp.where(first, value, terms[0])
-        while len(terms) > 1:
-            terms = [terms[i] + terms[i + 1] for i in range(0, len(terms), 2)]
-        value = terms[0] + swap(terms[0], "col", 1)
-        stride *= radix
+        here = jnp.where(first, value, terms[0]) + terms[1]
+        far = []
+        for cross in range(2):
+            pairs = [
+                (row * 2 + core, (row ^ 4 * stride) * 2 + (core ^ cross))
+                for row in range(rows)
+                for core in range(2)
+            ]
+            far.append(lax.ppermute(here, ("row", "col"), pairs))
+        value = (here + swap(here, "col", 1)) + (far[0] + far[1])
+        stride *= 8
     return value
 
 
@@ -46,13 +56,13 @@
     rows, cols = value.shape[0] >> len(order), value.shape[1]
     total = value.reshape([2] * len(order) + [rows, cols])
     left = sorted(order, reverse=True)
-    for bit in order:
+    for step, bit in enumerate(order):
         dim = left.index(bit)
         left.remove(bit)
         low = lax.index_in_dim(total, 0, dim, keepdims=False)
         high = lax.index_in_dim(total, 1, dim, keepdims=False)
         upper = bit_of(axis, bit) == 1
-        send = jnp.where(upper, low, high).astype(jnp.bfloat16)
+        send = jnp.where(upper, low, high).astype(LINK_TYPES[min(step, 2)])
         landed = swap(send, axis, 1 << bit)
         total = jnp.where(upper, high, low) + landed.astype(jnp.float32)
     return total
@@ -63,11 +73,11 @@
 
 
 def sum_and_share(value, axis, order, scale):
-    for bit in order[:-1]:
+    for step, bit in enumerate(order[:-1]):
         upper = bit_of(axis, bit) == 1
         half = value.shape[1] // 2
         low, high = value[:, :half], value[:, half:]
-        send = jnp.where(upper, low, high).astype(jnp.bfloat16)
+        send = jnp.where(upper, low, high).astype(LINK_TYPES[min(step, 2)])
         landed = swap(send, axis, 1 << bit)
         value = jnp.where(upper, high, low) + landed.astype(jnp.float32)
     landed = swap(value.astype(jnp.bfloat16), axis, 1 << order[-1])

time: 81.8 us -> 85.4 us (1.044)
  waiting for transfers between devices: 22.3 us -> 25.1 us
  starting transfers between devices: 44.5 us -> 45.4 us
    ppermute x0 -> x2, waiting for transfers between devices: none -> 4.32 us  [row_sum(): far.append(lax.ppermute(here, ('row', 'col'), pairs))]
    ppermute x0 -> x2, starting transfers between devices: none -> 4.31 us  [row_sum(): far.append(lax.ppermute(here, ('row', 'col'), pairs))]
    ppermute x4 -> x2, starting transfers between devices: 5.1 us -> 1.5 us  [row_sum(): terms.append(lax.ppermute(value, ('row', 'col'), pairs))]
    ppermute x34, waiting for transfers between devices: 19.6 us -> 17.9 us  [swap(): return lax.ppermute(value, axis, [(i, i ^ distance) for i in range(size)])]
    ppermute x4 -> x2, waiting for transfers between devices: 2.67 us -> 2.91 us  [row_sum(): terms.append(lax.ppermute(value, ('row', 'col'), pairs))]
  transfers between devices with their start and end apart: 38 -> 38, of which waited for: 19 -> 22; matrix products, arithmetic and copies ran while one was open for 3% -> 3% of each run, Pallas kernels for 2% -> 2%
where the time goes in v27:
time: 85.4 us; the launch traced here: 85.1 us
  starting transfers between devices  45.4 us (53%)
  waiting for transfers between devices  25.1 us (29%)
  Pallas kernels  8.67 us (10%)
  other arithmetic  2.1 us (2%)
  matrix products  1.77 us (2%)
  between operations  1.11 us (1%)
  local copies, waits for them, and re-layouts  1.05 us (1%)
    ppermute x34, starting transfers between devices, swap(): return lax.ppermute(value, axis, [(i, i ^ distance) for i in range(size)])  39.5 us
    ppermute x34, waiting for transfers between devices, swap(): return lax.ppermute(value, axis, [(i, i ^ distance) for i in range(size)])  17.9 us
    ppermute x2, waiting for transfers between devices, row_sum(): far.append(lax.ppermute(here, ('row', 'col'), pairs))  4.32 us
    ppermute x2, starting transfers between devices, row_sum(): far.append(lax.ppermute(here, ('row', 'col'), pairs))  4.31 us
    pallas_call x1, Pallas kernels, make_basis(): pl.pallas_call(functools.partial(basis_kernel, root_rows), out_shape=[jax...  4.1 us
    pallas_call x2, Pallas kernels, first_product(): pl.pallas_call(functools.partial(sketch_kernel, begin), out_shape=[jax.Sh...  4.07 us
    ppermute x2, waiting for transfers between devices, row_sum(): terms.append(lax.ppermute(value, ('row', 'col'), pairs))  2.91 us
    dot_general x4, matrix products, per_device(): lax.dot_general(activations[:, span], shared, (((1,), (1,)), ((), ())), p...  1.77 us
  transfers between devices with their start and end apart: 38, of which 22 were waited for; matrix products, arithmetic and copies ran while one was open for 3% of the time, Pallas kernels for 2%

profile of v27, /device:TPU:0, one launch (start us, length us, event | category | flops | bytes accessed | tf_op | source)
XLA Modules:
  0.0 85.1 jit_solution(16408584585253279864)
XLA Ops:
  0.7 0.9 %copy-done = bf16[512,128]{1,0:T(8,128)(2,1)S(1)} copy-done((bf16[512,128]{1,0:T(8,128)(2,1)S(1)}, bf16[512,128]{1,0:T(8,128)(2,1)}, u32[]{:S(2)}) %copy-start) | copy-done | bytes 131096
  1.6 2.1 %first_product.3 = (f32[128,1024]{1,0:T(8,128)S(1)}, f32[128,1024]{1,0:T(8,128)S(1)}) custom-call(bf16[512,128]{1,0:T(8,128)(2,1)S(1)} %copy-done, bf16[512,4096]{1,0:T(8,128)(2,1)} %slab_ref.5), custom_call_target="tpu_custom_call" | custom-call | flops 268435456 | bytes 2097152 | tf_op jit(solution)/shard_map/first_product/pallas_call | solution.py:127
  3.6 3.1 %collective-permute-start.15 = (bf16[128,512]{1,0:T(8,128)(2,1)S(1)}, bf16[128,512]{1,0:T(8,128)(2,1)S(1)}, u32[]{:S(2)}, u32[]{:S(2)}) collective-permute-start(bf16[128,512]{1,0:T(8,128)(2,1)S(1)} %select_convert_fusion.4), channel_id=1, source_target_pairs={{0,4},{2,6},{4,0},{6,2},{8,12},{10,14},{12,8},{14,10},{1,5},{3,7},... | collective-permute-start | bytes 393224 | tf_op jit(solution)/shard_map/ppermute | solution.py:19
  6.8 1.6 %collective-permute-start.10 = (bf16[128,512]{1,0:T(8,128)(2,1)S(1)}, bf16[128,512]{1,0:T(8,128)(2,1)S(1)}, u32[]{:S(2)}, u32[]{:S(2)}) collective-permute-start(bf16[128,512]{1,0:T(8,128)(2,1)S(1)} %select_convert_fusion.5), channel_id=1, source_target_pairs={{0,2},{2,0},{4,6},{6,4},{8,10},{10,8},{12,14},{14,12},{1,3},{3,1},... | collective-permute-start | bytes 393224 | tf_op jit(solution)/shard_map/ppermute | solution.py:19
  8.3 2.0 %first_product.2 = (f32[128,1024]{1,0:T(8,128)S(1)}, f32[128,1024]{1,0:T(8,128)S(1)}) custom-call(bf16[512,128]{1,0:T(8,128)(2,1)S(1)} %copy-done.1, bf16[512,4096]{1,0:T(8,128)(2,1)} %slab_ref.5), custom_call_target="tpu_custom_call" | custom-call | flops 268435456 | bytes 2097152 | tf_op jit(solution)/shard_map/first_product/pallas_call | solution.py:127
  11.2 2.0 %collective-permute-start.16 = (f32[128,256]{1,0:T(8,128)S(1)}, f32[128,256]{1,0:T(8,128)S(1)}, u32[]{:S(2)}, u32[]{:S(2)}) collective-permute-start(f32[128,256]{1,0:T(8,128)S(1)} %slice_select_fusion), channel_id=1, source_target_pairs={{0,2},{2,0},{4,6},{6,4},{8,10},{10,8},{12,14},{14,12},{1,3},{3,1},... | collective-permute-start | bytes 393224 | tf_op jit(solution)/shard_map/ppermute | solution.py:19
  13.3 1.6 %collective-permute-start.11 = (f32[128,256]{1,0:T(8,128)S(1)}, f32[128,256]{1,0:T(8,128)S(1)}, u32[]{:S(2)}, u32[]{:S(2)}) collective-permute-start(f32[128,256]{1,0:T(8,128)S(1)} %slice_select_fusion.1), channel_id=1, source_target_pairs={{0,4},{2,6},{4,0},{6,2},{8,12},{10,14},{12,8},{14,10},{1,5},{3,7},... | collective-permute-start | bytes 393224 | tf_op jit(solution)/shard_map/ppermute | solution.py:19
  14.9 1.6 %collective-permute-done.5 = bf16[128,512]{1,0:T(8,128)(2,1)S(1)} collective-permute-done((bf16[128,512]{1,0:T(8,128)(2,1)S(1)}, bf16[128,512]{1,0:T(8,128)(2,1)S(1)}, u32[]{:S(2)}, u32[]{:S(2)}) %collective-permute-start.5) | collective-permute-done | bytes 131104 | tf_op jit(solution)/shard_map/ppermute | solution.py:19
  16.6 0.8 collective-permute-start.6
  17.4 1.8 %collective-permute-start.1 = (f32[128,256]{1,0:T(8,128)S(1)}, f32[128,256]{1,0:T(8,128)S(1)}, u32[]{:S(2)}, u32[]{:S(2)}) collective-permute-start(f32[128,256]{1,0:T(8,128)S(1)} %slice_select_fusion.3), channel_id=1, source_target_pairs={{0,4},{2,6},{4,0},{6,2},{8,12},{10,14},{12,8},{14,10},{1,5},{3,7},... | collective-permute-start | bytes 393224 | tf_op jit(solution)/shard_map/ppermute | solution.py:19
  19.6 2.7 %collective-permute-start.17 = (bf16[128,256]{1,0:T(8,128)(2,1)S(1)}, bf16[128,256]{1,0:T(8,128)(2,1)S(1)}, u32[]{:S(2)}, u32[]{:S(2)}) collective-permute-start(bf16[128,256]{1,0:T(8,128)(2,1)S(1)} %get-tuple-element.30), channel_id=1, source_target_pairs={{0,8},{2,10},{4,12},{6,14},{8,0},{10,2},{12,4},{14,6},{1,9},{3,11}... | collective-permute-start | bytes 196616 | tf_op jit(solution)/shard_map/ppermute | solution.py:19
  22.8 2.7 %collective-permute-start.7 = (bf16[128,256]{1,0:T(8,128)(2,1)S(1)}, bf16[128,256]{1,0:T(8,128)(2,1)S(1)}, u32[]{:S(2)}, u32[]{:S(2)}) collective-permute-start(bf16[128,256]{1,0:T(8,128)(2,1)S(1)} %get-tuple-element.26), channel_id=1, source_target_pairs={{0,8},{2,10},{4,12},{6,14},{8,0},{10,2},{12,4},{14,6},{1,9},{3,11}... | collective-permute-start | bytes 196616 | tf_op jit(solution)/shard_map/ppermute | solution.py:19
  25.4 0.7 collective-permute-start.2
  26.1 1.3 %collective-permute-done.17 = bf16[128,256]{1,0:T(8,128)(2,1)S(1)} collective-permute-done((bf16[128,256]{1,0:T(8,128)(2,1)S(1)}, bf16[128,256]{1,0:T(8,128)(2,1)S(1)}, u32[]{:S(2)}, u32[]{:S(2)}) %collective-permute-start.17) | collective-permute-done | bytes 65568 | tf_op jit(solution)/shard_map/ppermute | solution.py:19
  27.5 0.9 %collective-permute-start.18 = (bf16[128,256]{1,0:T(8,128)(2,1)S(1)}, bf16[128,256]{1,0:T(8,128)(2,1)S(1)}, u32[]{:S(2)}, u32[]{:S(2)}) collective-permute-start(bf16[128,256]{1,0:T(8,128)(2,1)S(1)} %multiply_convert_fusion), channel_id=1, source_target_pairs={{0,2},{2,0},{4,6},{6,4},{8,10},{10,8},{12,14},{14,12},{1,3},{3,1},... | collective-permute-start | bytes 196616 | tf_op jit(solution)/shard_map/ppermute | solution.py:19
  28.4 1.7 %collective-permute-done.12 = bf16[128,256]{1,0:T(8,128)(2,1)S(1)} collective-permute-done((bf16[128,256]{1,0:T(8,128)(2,1)S(1)}, bf16[128,256]{1,0:T(8,128)(2,1)S(1)}, u32[]{:S(2)}, u32[]{:S(2)}) %collective-permute-start.12) | collective-permute-done | bytes 65568 | tf_op jit(solution)/shard_map/ppermute | solution.py:19
  30.8 0.9 %collective-permute-start.8 = (bf16[128,256]{1,0:T(8,128)(2,1)S(1)}, bf16[128,256]{1,0:T(8,128)(2,1)S(1)}, u32[]{:S(2)}, u32[]{:S(2)}) collective-permute-start(bf16[128,256]{1,0:T(8,128)(2,1)S(1)} %multiply_convert_fusion.2), channel_id=1, source_target_pairs={{0,2},{2,0},{4,6},{6,4},{8,10},{10,8},{12,14},{14,12},{1,3},{3,1},... | collective-permute-start | bytes 196616 | tf_op jit(solution)/shard_map/ppermute | solution.py:19
  32.2 1.0 %collective-permute-start.3 = (bf16[128,256]{1,0:T(8,128)(2,1)S(1)}, bf16[128,256]{1,0:T(8,128)(2,1)S(1)}, u32[]{:S(2)}, u32[]{:S(2)}) collective-permute-start(bf16[128,256]{1,0:T(8,128)(2,1)S(1)} %multiply_convert_fusion.3), channel_id=1, source_target_pairs={{0,4},{2,6},{4,0},{6,2},{8,12},{10,14},{12,8},{14,10},{1,5},{3,7},... | collective-permute-start | bytes 196616 | tf_op jit(solution)/shard_map/ppermute | solution.py:19
  33.2 1.2 %collective-permute-start.19 = (bf16[128,512]{1,0:T(8,128)(2,1)S(1)}, bf16[128,512]{1,0:T(8,128)(2,1)S(1)}, u32[]{:S(2)}, u32[]{:S(2)}) collective-permute-start(bf16[128,512]{1,0:T(8,128)(2,1)S(1)} %pad_maximum_fusion.4), channel_id=1, source_target_pairs={{0,4},{2,6},{4,0},{6,2},{8,12},{10,14},{12,8},{14,10},{1,5},{3,7},... | collective-permute-start | bytes 393224 | tf_op jit(solution)/shard_map/ppermute | solution.py:19
  34.4 0.7 collective-permute-done.13
  35.2 0.9 %collective-permute-start.14 = (bf16[128,512]{1,0:T(8,128)(2,1)S(1)}, bf16[128,512]{1,0:T(8,128)(2,1)S(1)}, u32[]{:S(2)}, u32[]{:S(2)}) collective-permute-start(bf16[128,512]{1,0:T(8,128)(2,1)S(1)} %pad_maximum_fusion.3), channel_id=1, source_target_pairs={{0,2},{2,0},{4,6},{6,4},{8,10},{10,8},{12,14},{14,12},{1,3},{3,1},... | collective-permute-start | bytes 393224 | tf_op jit(solution)/shard_map/ppermute | solution.py:19
  36.1 1.1 %collective-permute-start.9 = (bf16[128,512]{1,0:T(8,128)(2,1)S(1)}, bf16[128,512]{1,0:T(8,128)(2,1)S(1)}, u32[]{:S(2)}, u32[]{:S(2)}) collective-permute-start(bf16[128,512]{1,0:T(8,128)(2,1)S(1)} %pad_maximum_fusion.2), channel_id=1, source_target_pairs={{0,4},{2,6},{4,0},{6,2},{8,12},{10,14},{12,8},{14,10},{1,5},{3,7},... | collective-permute-start | bytes 393224 | tf_op jit(solution)/shard_map/ppermute | solution.py:19
  37.3 0.9 %collective-permute-start.4 = (bf16[128,512]{1,0:T(8,128)(2,1)S(1)}, bf16[128,512]{1,0:T(8,128)(2,1)S(1)}, u32[]{:S(2)}, u32[]{:S(2)}) collective-permute-start(bf16[128,512]{1,0:T(8,128)(2,1)S(1)} %pad_maximum_fusion.1), channel_id=1, source_target_pairs={{0,2},{2,0},{4,6},{6,4},{8,10},{10,8},{12,14},{14,12},{1,3},{3,1},... | collective-permute-start | bytes 393224 | tf_op jit(solution)/shard_map/ppermute | solution.py:19
  38.2 0.8 collective-permute-done.19
  39.5 0.7 collective-permute-done.14
  41.6 0.8 collective-permute-done.4
  43.0 1.5 %collective-permute-done.20.other_ref = f32[512,128]{1,0:T(8,128)S(1)} collective-permute-done((f32[512,128]{1,0:T(8,128)S(1)}, f32[512,128]{1,0:T(8,128)S(1)}, u32[]{:S(2)}, u32[]{:S(2)}) %collective-permute-start.20) | collective-permute-done | bytes 262176 | tf_op jit(solution)/shard_map/ppermute | solution.py:19
  45.0 0.8 collective-permute-start.22
  45.8 0.7 collective-permute-start.21
  46.5 2.9 %collective-permute-done.22 = f32[72,128]{1,0:T(8,128)S(1)} collective-permute-done((f32[72,128]{1,0:T(8,128)S(1)}, f32[72,128]{1,0:T(8,128)S(1)}, u32[]{:S(2)}, u32[]{:S(2)}) %collective-permute-start.22) | collective-permute-done | bytes 36896 | tf_op jit(solution)/shard_map/ppermute | solution.py:40
  49.4 3.8 %collective-permute-start.25 = (f32[72,128]{1,0:T(8,128)S(1)}, f32[72,128]{1,0:T(8,128)S(1)}, u32[]{:S(2)}, u32[]{:S(2)}) collective-permute-start(f32[72,128]{1,0:T(8,128)S(1)} %select_add_fusion.4), channel_id=1, source_target_pairs={{0,9},{1,8},{2,11},{3,10},{4,13},{5,12},{6,15},{7,14},{8,1},{9,0},... | collective-permute-start | bytes 110600 | tf_op jit(solution)/shard_map/ppermute | solution.py:49
  53.7 1.1 %collective-permute-done.25 = f32[72,128]{1,0:T(8,128)S(1)} collective-permute-done((f32[72,128]{1,0:T(8,128)S(1)}, f32[72,128]{1,0:T(8,128)S(1)}, u32[]{:S(2)}, u32[]{:S(2)}) %collective-permute-start.25) | collective-permute-done | bytes 36896 | tf_op jit(solution)/shard_map/ppermute | solution.py:49
  54.8 3.2 %collective-permute-done.24 = f32[72,128]{1,0:T(8,128)S(1)} collective-permute-done((f32[72,128]{1,0:T(8,128)S(1)}, f32[72,128]{1,0:T(8,128)S(1)}, u32[]{:S(2)}, u32[]{:S(2)}) %collective-permute-start.24) | collective-permute-done | bytes 36896 | tf_op jit(solution)/shard_map/ppermute | solution.py:49
  58.1 4.1 %make_basis.1 = (f32[512,128]{1,0:T(8,128)}, f32[128,1024]{1,0:T(8,128)S(1)}, f32[128,1024]{1,0:T(8,128)S(1)}, f32[128,1024]{1,0:T(8,128)S(1)}, f32[128,1024]{1,0:T(8,128)S(1)}) custom-call(f32[72,128]{1,0:T(8,128)S(1)} %add_add_fusion.gram_ref, f32[128,512]{1,0:T(8,128)S(1)} %get-tuple-element.18.sketch_ref, bf16[512,4096]{1,0:T(8,128)(2,1)} %slab_ref.5), custom_call_target="tpu_custom_call" | custom-call | tf_op jit(solution)/shard_map/make_basis/pallas_call | solution.py:289
  62.3 1.8 %collective-permute-start.26 = (bf16[2,2,16,1024]{3,2,0,1:T(8,128)(2,1)S(1)}, bf16[2,2,16,1024]{3,2,0,1:T(8,128)(2,1)S(1)}, u32[]{:S(2)}, u32[]{:S(2)}) collective-permute-start(bf16[2,2,16,1024]{3,2,0,1:T(8,128)(2,1)S(1)} %fusion.22), channel_id=1, source_target_pairs={{0,2},{2,0},{4,6},{6,4},{8,10},{10,8},{12,14},{14,12},{1,3},{3,1},... | collective-permute-start | bytes 393224 | tf_op jit(solution)/shard_map/ppermute | solution.py:19
  64.7 1.4 %collective-permute-start.32 = (bf16[2,2,16,1024]{3,2,0,1:T(8,128)(2,1)S(1)}, bf16[2,2,16,1024]{3,2,0,1:T(8,128)(2,1)S(1)}, u32[]{:S(2)}, u32[]{:S(2)}) collective-permute-start(bf16[2,2,16,1024]{3,2,0,1:T(8,128)(2,1)S(1)} %fusion.24), channel_id=1, source_target_pairs={{0,2},{2,0},{4,6},{6,4},{8,10},{10,8},{12,14},{14,12},{1,3},{3,1},... | collective-permute-start | bytes 393224 | tf_op jit(solution)/shard_map/ppermute | solution.py:19
  66.8 1.3 %collective-permute-done.26 = bf16[2,2,16,1024]{3,2,0,1:T(8,128)(2,1)S(1)} collective-permute-done((bf16[2,2,16,1024]{3,2,0,1:T(8,128)(2,1)S(1)}, bf16[2,2,16,1024]{3,2,0,1:T(8,128)(2,1)S(1)}, u32[]{:S(2)}, u32[]{:S(2)}) %collective-permute-start.26) | collective-permute-done | bytes 131104 | tf_op jit(solution)/shard_map/ppermute | solution.py:19
  68.2 1.3 %collective-permute-start.27 = (f32[2,16,1024]{2,1,0:T(8,128)S(1)}, f32[2,16,1024]{2,1,0:T(8,128)S(1)}, u32[]{:S(2)}, u32[]{:S(2)}) collective-permute-start(f32[2,16,1024]{2,1,0:T(8,128)S(1)} %select_bitcast_fusion.3), channel_id=1, source_target_pairs={{0,4},{2,6},{4,0},{6,2},{8,12},{10,14},{12,8},{14,10},{1,5},{3,7},... | collective-permute-start | bytes 393224 | tf_op jit(solution)/shard_map/ppermute | solution.py:19
  69.6 0.9 %collective-permute-done.29 = bf16[2,2,16,1024]{3,2,0,1:T(8,128)(2,1)S(1)} collective-permute-done((bf16[2,2,16,1024]{3,2,0,1:T(8,128)(2,1)S(1)}, bf16[2,2,16,1024]{3,2,0,1:T(8,128)(2,1)S(1)}, u32[]{:S(2)}, u32[]{:S(2)}) %collective-permute-start.29) | collective-permute-done | bytes 131104 | tf_op jit(solution)/shard_map/ppermute | solution.py:19
  71.1 1.6 %collective-permute-start.33 = (f32[2,16,1024]{2,1,0:T(8,128)S(1)}, f32[2,16,1024]{2,1,0:T(8,128)S(1)}, u32[]{:S(2)}, u32[]{:S(2)}) collective-permute-start(f32[2,16,1024]{2,1,0:T(8,128)S(1)} %select_bitcast_fusion.1), channel_id=1, source_target_pairs={{0,4},{2,6},{4,0},{6,2},{8,12},{10,14},{12,8},{14,10},{1,5},{3,7},... | collective-permute-start | bytes 393224 | tf_op jit(solution)/shard_map/ppermute | solution.py:19
  73.9 1.3 %collective-permute-done.27 = f32[2,16,1024]{2,1,0:T(8,128)S(1)} collective-permute-done((f32[2,16,1024]{2,1,0:T(8,128)S(1)}, f32[2,16,1024]{2,1,0:T(8,128)S(1)}, u32[]{:S(2)}, u32[]{:S(2)}) %collective-permute-start.27) | collective-permute-done | bytes 131104 | tf_op jit(solution)/shard_map/ppermute | solution.py:19
  75.2 1.1 %collective-permute-start.28 = (bf16[16,1024]{1,0:T(8,128)(2,1)S(1)}, bf16[16,1024]{1,0:T(8,128)(2,1)S(1)}, u32[]{:S(2)}, u32[]{:S(2)}) collective-permute-start(bf16[16,1024]{1,0:T(8,128)(2,1)S(1)} %fusion.30), channel_id=1, source_target_pairs={{0,8},{2,10},{4,12},{6,14},{8,0},{10,2},{12,4},{14,6},{1,9},{3,11}... | collective-permute-start | bytes 98312 | tf_op jit(solution)/shard_map/ppermute | solution.py:19
  76.4 1.9 %collective-permute-start.31 = (bf16[16,1024]{1,0:T(8,128)(2,1)S(1)}, bf16[16,1024]{1,0:T(8,128)(2,1)S(1)}, u32[]{:S(2)}, u32[]{:S(2)}) collective-permute-start(bf16[16,1024]{1,0:T(8,128)(2,1)S(1)} %fusion.31), channel_id=1, source_target_pairs={{0,8},{2,10},{4,12},{6,14},{8,0},{10,2},{12,4},{14,6},{1,9},{3,11}... | collective-permute-start | bytes 98312 | tf_op jit(solution)/shard_map/ppermute | solution.py:19
  78.4 1.1 %collective-permute-start.34 = (bf16[16,1024]{1,0:T(8,128)(2,1)S(1)}, bf16[16,1024]{1,0:T(8,128)(2,1)S(1)}, u32[]{:S(2)}, u32[]{:S(2)}) collective-permute-start(bf16[16,1024]{1,0:T(8,128)(2,1)S(1)} %fusion.32), channel_id=1, source_target_pairs={{0,8},{2,10},{4,12},{6,14},{8,0},{10,2},{12,4},{14,6},{1,9},{3,11}... | collective-permute-start | bytes 98312 | tf_op jit(solution)/shard_map/ppermute | solution.py:19
  79.5 1.9 %collective-permute-start.37 = (bf16[16,1024]{1,0:T(8,128)(2,1)S(1)}, bf16[16,1024]{1,0:T(8,128)(2,1)S(1)}, u32[]{:S(2)}, u32[]{:S(2)}) collective-permute-start(bf16[16,1024]{1,0:T(8,128)(2,1)S(1)} %fusion.33), channel_id=1, source_target_pairs={{0,8},{2,10},{4,12},{6,14},{8,0},{10,2},{12,4},{14,6},{1,9},{3,11}... | collective-permute-start | bytes 98312 | tf_op jit(solution)/shard_map/ppermute | solution.py:19
  81.5 1.7 %collective-permute-done.34 = bf16[16,1024]{1,0:T(8,128)(2,1)S(1)} collective-permute-done((bf16[16,1024]{1,0:T(8,128)(2,1)S(1)}, bf16[16,1024]{1,0:T(8,128)(2,1)S(1)}, u32[]{:S(2)}, u32[]{:S(2)}) %collective-permute-start.34) | collective-permute-done | bytes 32800 | tf_op jit(solution)/shard_map/ppermute | solution.py:19
  83.3 1.2 %collective-permute-done.37 = bf16[16,1024]{1,0:T(8,128)(2,1)S(1)} collective-permute-done((bf16[16,1024]{1,0:T(8,128)(2,1)S(1)}, bf16[16,1024]{1,0:T(8,128)(2,1)S(1)}, u32[]{:S(2)}, u32[]{:S(2)}) %collective-permute-start.37) | collective-permute-done | bytes 32800 | tf_op jit(solution)/shard_map/ppermute | solution.py:19
  84.4 0.7 pad_maximum_fusion
  (105 shorter events, 10.5 us)
Async XLA Ops:
  0.6 0.9 %copy-start = (bf16[512,128]{1,0:T(8,128)(2,1)S(1)}, bf16[512,128]{1,0:T(8,128)(2,1)}, u32[]{:S(2)}) copy-start(bf16[512,128]{1,0:T(8,128)(2,1)} %start_ref.3) | copy-start | bytes 393220
  1.6 6.8 %copy-start.1 = (bf16[512,128]{1,0:T(8,128)(2,1)S(1)}, bf16[512,128]{1,0:T(8,128)(2,1)}, u32[]{:S(2)}) copy-start(bf16[512,128]{1,0:T(8,128)(2,1)} %start_ref.3) | copy-start | bytes 393220
  3.6 7.5 %collective-permute-start.15 = (bf16[128,512]{1,0:T(8,128)(2,1)S(1)}, bf16[128,512]{1,0:T(8,128)(2,1)S(1)}, u32[]{:S(2)}, u32[]{:S(2)}) collective-permute-start(bf16[128,512]{1,0:T(8,128)(2,1)S(1)} %select_convert_fusion.4), channel_id=1, source_target_pairs={{0,4},{2,6},{4,0},{6,2},{8,12},{10,14},{12,8},{14,10},{1,5},{3,7},... | collective-permute-start | bytes 393224 | tf_op jit(solution)/shard_map/ppermute | solution.py:19
  6.8 6.4 %collective-permute-start.10 = (bf16[128,512]{1,0:T(8,128)(2,1)S(1)}, bf16[128,512]{1,0:T(8,128)(2,1)S(1)}, u32[]{:S(2)}, u32[]{:S(2)}) collective-permute-start(bf16[128,512]{1,0:T(8,128)(2,1)S(1)} %select_convert_fusion.5), channel_id=1, source_target_pairs={{0,2},{2,0},{4,6},{6,4},{8,10},{10,8},{12,14},{14,12},{1,3},{3,1},... | collective-permute-start | bytes 393224 | tf_op jit(solution)/shard_map/ppermute | solution.py:19
  10.4 6.1 %collective-permute-start.5 = (bf16[128,512]{1,0:T(8,128)(2,1)S(1)}, bf16[128,512]{1,0:T(8,128)(2,1)S(1)}, u32[]{:S(2)}, u32[]{:S(2)}) collective-permute-start(bf16[128,512]{1,0:T(8,128)(2,1)S(1)} %select_convert_fusion.6), channel_id=1, source_target_pairs={{0,4},{2,6},{4,0},{6,2},{8,12},{10,14},{12,8},{14,10},{1,5},{3,7},... | collective-permute-start | bytes 393224 | tf_op jit(solution)/shard_map/ppermute | solution.py:19
  10.9 6.4 %collective-permute-start = (bf16[128,512]{1,0:T(8,128)(2,1)S(1)}, bf16[128,512]{1,0:T(8,128)(2,1)S(1)}, u32[]{:S(2)}, u32[]{:S(2)}) collective-permute-start(bf16[128,512]{1,0:T(8,128)(2,1)S(1)} %select_convert_fusion.7), channel_id=1, source_target_pairs={{0,2},{2,0},{4,6},{6,4},{8,10},{10,8},{12,14},{14,12},{1,3},{3,1},... | collective-permute-start | bytes 393224 | tf_op jit(solution)/shard_map/ppermute | solution.py:19
  11.2 8.4 %collective-permute-start.16 = (f32[128,256]{1,0:T(8,128)S(1)}, f32[128,256]{1,0:T(8,128)S(1)}, u32[]{:S(2)}, u32[]{:S(2)}) collective-permute-start(f32[128,256]{1,0:T(8,128)S(1)} %slice_select_fusion), channel_id=1, source_target_pairs={{0,2},{2,0},{4,6},{6,4},{8,10},{10,8},{12,14},{14,12},{1,3},{3,1},... | collective-permute-start | bytes 393224 | tf_op jit(solution)/shard_map/ppermute | solution.py:19
  13.2 25.8 %copy-start.2 = (bf16[512,4096]{1,0:T(8,128)(2,1)S(1)}, bf16[512,4096]{1,0:T(8,128)(2,1)}, u32[]{:S(2)}) copy-start(bf16[512,4096]{1,0:T(8,128)(2,1)} %slab_ref.5) | copy-start | bytes 12582916
  13.3 9.0 %collective-permute-start.11 = (f32[128,256]{1,0:T(8,128)S(1)}, f32[128,256]{1,0:T(8,128)S(1)}, u32[]{:S(2)}, u32[]{:S(2)}) collective-permute-start(f32[128,256]{1,0:T(8,128)S(1)} %slice_select_fusion.1), channel_id=1, source_target_pairs={{0,4},{2,6},{4,0},{6,2},{8,12},{10,14},{12,8},{14,10},{1,5},{3,7},... | collective-permute-start | bytes 393224 | tf_op jit(solution)/shard_map/ppermute | solution.py:19
  16.6 6.2 %collective-permute-start.6 = (f32[128,256]{1,0:T(8,128)S(1)}, f32[128,256]{1,0:T(8,128)S(1)}, u32[]{:S(2)}, u32[]{:S(2)}) collective-permute-start(f32[128,256]{1,0:T(8,128)S(1)} %slice_select_fusion.2), channel_id=1, source_target_pairs={{0,2},{2,0},{4,6},{6,4},{8,10},{10,8},{12,14},{14,12},{1,3},{3,1},... | collective-permute-start | bytes 393224 | tf_op jit(solution)/shard_map/ppermute | solution.py:19
  17.4 8.0 %collective-permute-start.1 = (f32[128,256]{1,0:T(8,128)S(1)}, f32[128,256]{1,0:T(8,128)S(1)}, u32[]{:S(2)}, u32[]{:S(2)}) collective-permute-start(f32[128,256]{1,0:T(8,128)S(1)} %slice_select_fusion.3), channel_id=1, source_target_pairs={{0,4},{2,6},{4,0},{6,2},{8,12},{10,14},{12,8},{14,10},{1,5},{3,7},... | collective-permute-start | bytes 393224 | tf_op jit(solution)/shard_map/ppermute | solution.py:19
  19.6 7.8 %collective-permute-start.17 = (bf16[128,256]{1,0:T(8,128)(2,1)S(1)}, bf16[128,256]{1,0:T(8,128)(2,1)S(1)}, u32[]{:S(2)}, u32[]{:S(2)}) collective-permute-start(bf16[128,256]{1,0:T(8,128)(2,1)S(1)} %get-tuple-element.30), channel_id=1, source_target_pairs={{0,8},{2,10},{4,12},{6,14},{8,0},{10,2},{12,4},{14,6},{1,9},{3,11}... | collective-permute-start | bytes 196616 | tf_op jit(solution)/shard_map/ppermute | solution.py:19
  22.3 7.8 %collective-permute-start.12 = (bf16[128,256]{1,0:T(8,128)(2,1)S(1)}, bf16[128,256]{1,0:T(8,128)(2,1)S(1)}, u32[]{:S(2)}, u32[]{:S(2)}) collective-permute-start(bf16[128,256]{1,0:T(8,128)(2,1)S(1)} %get-tuple-element.28), channel_id=1, source_target_pairs={{0,8},{2,10},{4,12},{6,14},{8,0},{10,2},{12,4},{14,6},{1,9},{3,11}... | collective-permute-start | bytes 196616 | tf_op jit(solution)/shard_map/ppermute | solution.py:19
  22.8 8.0 %collective-permute-start.7 = (bf16[128,256]{1,0:T(8,128)(2,1)S(1)}, bf16[128,256]{1,0:T(8,128)(2,1)S(1)}, u32[]{:S(2)}, u32[]{:S(2)}) collective-permute-start(bf16[128,256]{1,0:T(8,128)(2,1)S(1)} %get-tuple-element.26), channel_id=1, source_target_pairs={{0,8},{2,10},{4,12},{6,14},{8,0},{10,2},{12,4},{14,6},{1,9},{3,11}... | collective-permute-start | bytes 196616 | tf_op jit(solution)/shard_map/ppermute | solution.py:19
  25.4 6.7 %collective-permute-start.2 = (bf16[128,256]{1,0:T(8,128)(2,1)S(1)}, bf16[128,256]{1,0:T(8,128)(2,1)S(1)}, u32[]{:S(2)}, u32[]{:S(2)}) collective-permute-start(bf16[128,256]{1,0:T(8,128)(2,1)S(1)} %get-tuple-element.24), channel_id=1, source_target_pairs={{0,8},{2,10},{4,12},{6,14},{8,0},{10,2},{12,4},{14,6},{1,9},{3,11}... | collective-permute-start | bytes 196616 | tf_op jit(solution)/shard_map/ppermute | solution.py:19
  27.5 5.7 %collective-permute-start.18 = (bf16[128,256]{1,0:T(8,128)(2,1)S(1)}, bf16[128,256]{1,0:T(8,128)(2,1)S(1)}, u32[]{:S(2)}, u32[]{:S(2)}) collective-permute-start(bf16[128,256]{1,0:T(8,128)(2,1)S(1)} %multiply_convert_fusion), channel_id=1, source_target_pairs={{0,2},{2,0},{4,6},{6,4},{8,10},{10,8},{12,14},{14,12},{1,3},{3,1},... | collective-permute-start | bytes 196616 | tf_op jit(solution)/shard_map/ppermute | solution.py:19
  30.1 5.0 %collective-permute-start.13 = (bf16[128,256]{1,0:T(8,128)(2,1)S(1)}, bf16[128,256]{1,0:T(8,128)(2,1)S(1)}, u32[]{:S(2)}, u32[]{:S(2)}) collective-permute-start(bf16[128,256]{1,0:T(8,128)(2,1)S(1)} %multiply_convert_fusion.1), channel_id=1, source_target_pairs={{0,4},{2,6},{4,0},{6,2},{8,12},{10,14},{12,8},{14,10},{1,5},{3,7},... | collective-permute-start | bytes 196616 | tf_op jit(solution)/shard_map/ppermute | solution.py:19
  30.8 5.2 %collective-permute-start.8 = (bf16[128,256]{1,0:T(8,128)(2,1)S(1)}, bf16[128,256]{1,0:T(8,128)(2,1)S(1)}, u32[]{:S(2)}, u32[]{:S(2)}) collective-permute-start(bf16[128,256]{1,0:T(8,128)(2,1)S(1)} %multiply_convert_fusion.2), channel_id=1, source_target_pairs={{0,2},{2,0},{4,6},{6,4},{8,10},{10,8},{12,14},{14,12},{1,3},{3,1},... | collective-permute-start | bytes 196616 | tf_op jit(solution)/shard_map/ppermute | solution.py:19
  32.2 5.1 %collective-permute-start.3 = (bf16[128,256]{1,0:T(8,128)(2,1)S(1)}, bf16[128,256]{1,0:T(8,128)(2,1)S(1)}, u32[]{:S(2)}, u32[]{:S(2)}) collective-permute-start(bf16[128,256]{1,0:T(8,128)(2,1)S(1)} %multiply_convert_fusion.3), channel_id=1, source_target_pairs={{0,4},{2,6},{4,0},{6,2},{8,12},{10,14},{12,8},{14,10},{1,5},{3,7},... | collective-permute-start | bytes 196616 | tf_op jit(solution)/shard_map/ppermute | solution.py:19
  33.2 5.8 %collective-permute-start.19 = (bf16[128,512]{1,0:T(8,128)(2,1)S(1)}, bf16[128,512]{1,0:T(8,128)(2,1)S(1)}, u32[]{:S(2)}, u32[]{:S(2)}) collective-permute-start(bf16[128,512]{1,0:T(8,128)(2,1)S(1)} %pad_maximum_fusion.4), channel_id=1, source_target_pairs={{0,4},{2,6},{4,0},{6,2},{8,12},{10,14},{12,8},{14,10},{1,5},{3,7},... | collective-permute-start | bytes 393224 | tf_op jit(solution)/shard_map/ppermute | solution.py:19
  35.2 5.0 %collective-permute-start.14 = (bf16[128,512]{1,0:T(8,128)(2,1)S(1)}, bf16[128,512]{1,0:T(8,128)(2,1)S(1)}, u32[]{:S(2)}, u32[]{:S(2)}) collective-permute-start(bf16[128,512]{1,0:T(8,128)(2,1)S(1)} %pad_maximum_fusion.3), channel_id=1, source_target_pairs={{0,2},{2,0},{4,6},{6,4},{8,10},{10,8},{12,14},{14,12},{1,3},{3,1},... | collective-permute-start | bytes 393224 | tf_op jit(solution)/shard_map/ppermute | solution.py:19
  36.1 5.0 %collective-permute-start.9 = (bf16[128,512]{1,0:T(8,128)(2,1)S(1)}, bf16[128,512]{1,0:T(8,128)(2,1)S(1)}, u32[]{:S(2)}, u32[]{:S(2)}) collective-permute-start(bf16[128,512]{1,0:T(8,128)(2,1)S(1)} %pad_maximum_fusion.2), channel_id=1, source_target_pairs={{0,4},{2,6},{4,0},{6,2},{8,12},{10,14},{12,8},{14,10},{1,5},{3,7},... | collective-permute-start | bytes 393224 | tf_op jit(solution)/shard_map/ppermute | solution.py:19
  37.3 5.0 %collective-permute-start.4 = (bf16[128,512]{1,0:T(8,128)(2,1)S(1)}, bf16[128,512]{1,0:T(8,128)(2,1)S(1)}, u32[]{:S(2)}, u32[]{:S(2)}) collective-permute-start(bf16[128,512]{1,0:T(8,128)(2,1)S(1)} %pad_maximum_fusion.1), channel_id=1, source_target_pairs={{0,2},{2,0},{4,6},{6,4},{8,10},{10,8},{12,14},{14,12},{1,3},{3,1},... | collective-permute-start | bytes 393224 | tf_op jit(solution)/shard_map/ppermute | solution.py:19
  42.9 1.6 %collective-permute-start.20 = (f32[512,128]{1,0:T(8,128)S(1)}, f32[512,128]{1,0:T(8,128)S(1)}, u32[]{:S(2)}, u32[]{:S(2)}) collective-permute-start(f32[512,128]{1,0:T(8,128)S(1)} %fusion.2.mine_ref), channel_id=1, source_target_pairs={{0,1},{1,0},{2,3},{3,2},{4,5},{5,4},{6,7},{7,6},{8,9},{9,8},{10,11... | collective-permute-start | bytes 786440 | tf_op jit(solution)/shard_map/ppermute | solution.py:19
  45.0 4.4 %collective-permute-start.22 = (f32[72,128]{1,0:T(8,128)S(1)}, f32[72,128]{1,0:T(8,128)S(1)}, u32[]{:S(2)}, u32[]{:S(2)}) collective-permute-start(f32[72,128]{1,0:T(8,128)S(1)} %get-tuple-element.17), channel_id=1, source_target_pairs={{0,2},{1,7},{2,0},{3,5},{4,6},{5,3},{6,4},{7,1},{8,10},{9,15},{10,... | collective-permute-start | bytes 110600 | tf_op jit(solution)/shard_map/ppermute | solution.py:40
  45.8 3.6 %collective-permute-start.21 = (f32[72,128]{1,0:T(8,128)S(1)}, f32[72,128]{1,0:T(8,128)S(1)}, u32[]{:S(2)}, u32[]{:S(2)}) collective-permute-start(f32[72,128]{1,0:T(8,128)S(1)} %get-tuple-element.17), channel_id=1, source_target_pairs={{1,5},{3,7},{5,1},{7,3},{9,13},{11,15},{13,9},{15,11},{17,21},{19,... | collective-permute-start | bytes 110600 | tf_op jit(solution)/shard_map/ppermute | solution.py:40
  49.4 5.4 %collective-permute-start.25 = (f32[72,128]{1,0:T(8,128)S(1)}, f32[72,128]{1,0:T(8,128)S(1)}, u32[]{:S(2)}, u32[]{:S(2)}) collective-permute-start(f32[72,128]{1,0:T(8,128)S(1)} %select_add_fusion.4), channel_id=1, source_target_pairs={{0,9},{1,8},{2,11},{3,10},{4,13},{5,12},{6,15},{7,14},{8,1},{9,0},... | collective-permute-start | bytes 110600 | tf_op jit(solution)/shard_map/ppermute | solution.py:49
  53.2 4.9 %collective-permute-start.24 = (f32[72,128]{1,0:T(8,128)S(1)}, f32[72,128]{1,0:T(8,128)S(1)}, u32[]{:S(2)}, u32[]{:S(2)}) collective-permute-start(f32[72,128]{1,0:T(8,128)S(1)} %select_add_fusion.4), channel_id=1, source_target_pairs={{0,8},{1,9},{2,10},{3,11},{4,12},{5,13},{6,14},{7,15},{8,0},{9,1},... | collective-permute-start | bytes 110600 | tf_op jit(solution)/shard_map/ppermute | solution.py:49
  53.7 4.3 %collective-permute-start.23 = (f32[72,128]{1,0:T(8,128)S(1)}, f32[72,128]{1,0:T(8,128)S(1)}, u32[]{:S(2)}, u32[]{:S(2)}) collective-permute-start(f32[72,128]{1,0:T(8,128)S(1)} %select_add_fusion.4), channel_id=1, source_target_pairs={{0,1},{1,0},{2,3},{3,2},{4,5},{5,4},{6,7},{7,6},{8,9},{9,8},{10,11... | collective-permute-start | bytes 110600 | tf_op jit(solution)/shard_map/ppermute | solution.py:19
  62.3 5.9 %collective-permute-start.26 = (bf16[2,2,16,1024]{3,2,0,1:T(8,128)(2,1)S(1)}, bf16[2,2,16,1024]{3,2,0,1:T(8,128)(2,1)S(1)}, u32[]{:S(2)}, u32[]{:S(2)}) collective-permute-start(bf16[2,2,16,1024]{3,2,0,1:T(8,128)(2,1)S(1)} %fusion.22), channel_id=1, source_target_pairs={{0,2},{2,0},{4,6},{6,4},{8,10},{10,8},{12,14},{14,12},{1,3},{3,1},... | collective-permute-start | bytes 393224 | tf_op jit(solution)/shard_map/ppermute | solution.py:19
  64.2 6.3 %collective-permute-start.29 = (bf16[2,2,16,1024]{3,2,0,1:T(8,128)(2,1)S(1)}, bf16[2,2,16,1024]{3,2,0,1:T(8,128)(2,1)S(1)}, u32[]{:S(2)}, u32[]{:S(2)}) collective-permute-start(bf16[2,2,16,1024]{3,2,0,1:T(8,128)(2,1)S(1)} %fusion.23), channel_id=1, source_target_pairs={{0,4},{2,6},{4,0},{6,2},{8,12},{10,14},{12,8},{14,10},{1,5},{3,7},... | collective-permute-start | bytes 393224 | tf_op jit(solution)/shard_map/ppermute | solution.py:19
  64.7 6.4 %collective-permute-start.32 = (bf16[2,2,16,1024]{3,2,0,1:T(8,128)(2,1)S(1)}, bf16[2,2,16,1024]{3,2,0,1:T(8,128)(2,1)S(1)}, u32[]{:S(2)}, u32[]{:S(2)}) collective-permute-start(bf16[2,2,16,1024]{3,2,0,1:T(8,128)(2,1)S(1)} %fusion.24), channel_id=1, source_target_pairs={{0,2},{2,0},{4,6},{6,4},{8,10},{10,8},{12,14},{14,12},{1,3},{3,1},... | collective-permute-start | bytes 393224 | tf_op jit(solution)/shard_map/ppermute | solution.py:19
  66.2 7.1 %collective-permute-start.35 = (bf16[2,2,16,1024]{3,2,0,1:T(8,128)(2,1)S(1)}, bf16[2,2,16,1024]{3,2,0,1:T(8,128)(2,1)S(1)}, u32[]{:S(2)}, u32[]{:S(2)}) collective-permute-start(bf16[2,2,16,1024]{3,2,0,1:T(8,128)(2,1)S(1)} %fusion.25), channel_id=1, source_target_pairs={{0,4},{2,6},{4,0},{6,2},{8,12},{10,14},{12,8},{14,10},{1,5},{3,7},... | collective-permute-start | bytes 393224 | tf_op jit(solution)/shard_map/ppermute | solution.py:19
  68.2 6.9 %collective-permute-start.27 = (f32[2,16,1024]{2,1,0:T(8,128)S(1)}, f32[2,16,1024]{2,1,0:T(8,128)S(1)}, u32[]{:S(2)}, u32[]{:S(2)}) collective-permute-start(f32[2,16,1024]{2,1,0:T(8,128)S(1)} %select_bitcast_fusion.3), channel_id=1, source_target_pairs={{0,4},{2,6},{4,0},{6,2},{8,12},{10,14},{12,8},{14,10},{1,5},{3,7},... | collective-permute-start | bytes 393224 | tf_op jit(solution)/shard_map/ppermute | solution.py:19
  70.6 5.8 %collective-permute-start.30 = (f32[2,16,1024]{2,1,0:T(8,128)S(1)}, f32[2,16,1024]{2,1,0:T(8,128)S(1)}, u32[]{:S(2)}, u32[]{:S(2)}) collective-permute-start(f32[2,16,1024]{2,1,0:T(8,128)S(1)} %select_bitcast_fusion.2), channel_id=1, source_target_pairs={{0,2},{2,0},{4,6},{6,4},{8,10},{10,8},{12,14},{14,12},{1,3},{3,1},... | collective-permute-start | bytes 393224 | tf_op jit(solution)/shard_map/ppermute | solution.py:19
  71.1 7.2 %collective-permute-start.33 = (f32[2,16,1024]{2,1,0:T(8,128)S(1)}, f32[2,16,1024]{2,1,0:T(8,128)S(1)}, u32[]{:S(2)}, u32[]{:S(2)}) collective-permute-start(f32[2,16,1024]{2,1,0:T(8,128)S(1)} %select_bitcast_fusion.1), channel_id=1, source_target_pairs={{0,4},{2,6},{4,0},{6,2},{8,12},{10,14},{12,8},{14,10},{1,5},{3,7},... | collective-permute-start | bytes 393224 | tf_op jit(solution)/shard_map/ppermute | solution.py:19
  73.4 6.1 %collective-permute-start.36 = (f32[2,16,1024]{2,1,0:T(8,128)S(1)}, f32[2,16,1024]{2,1,0:T(8,128)S(1)}, u32[]{:S(2)}, u32[]{:S(2)}) collective-permute-start(f32[2,16,1024]{2,1,0:T(8,128)S(1)} %select_bitcast_fusion), channel_id=1, source_target_pairs={{0,2},{2,0},{4,6},{6,4},{8,10},{10,8},{12,14},{14,12},{1,3},{3,1},... | collective-permute-start | bytes 393224 | tf_op jit(solution)/shard_map/ppermute | solution.py:19
  75.2 6.3 %collective-permute-start.28 = (bf16[16,1024]{1,0:T(8,128)(2,1)S(1)}, bf16[16,1024]{1,0:T(8,128)(2,1)S(1)}, u32[]{:S(2)}, u32[]{:S(2)}) collective-permute-start(bf16[16,1024]{1,0:T(8,128)(2,1)S(1)} %fusion.30), channel_id=1, source_target_pairs={{0,8},{2,10},{4,12},{6,14},{8,0},{10,2},{12,4},{14,6},{1,9},{3,11}... | collective-permute-start | bytes 98312 | tf_op jit(solution)/shard_map/ppermute | solution.py:19
  76.4 5.1 %collective-permute-start.31 = (bf16[16,1024]{1,0:T(8,128)(2,1)S(1)}, bf16[16,1024]{1,0:T(8,128)(2,1)S(1)}, u32[]{:S(2)}, u32[]{:S(2)}) collective-permute-start(bf16[16,1024]{1,0:T(8,128)(2,1)S(1)} %fusion.31), channel_id=1, source_target_pairs={{0,8},{2,10},{4,12},{6,14},{8,0},{10,2},{12,4},{14,6},{1,9},{3,11}... | collective-permute-start | bytes 98312 | tf_op jit(solution)/shard_map/ppermute | solution.py:19
  78.4 4.9 %collective-permute-start.34 = (bf16[16,1024]{1,0:T(8,128)(2,1)S(1)}, bf16[16,1024]{1,0:T(8,128)(2,1)S(1)}, u32[]{:S(2)}, u32[]{:S(2)}) collective-permute-start(bf16[16,1024]{1,0:T(8,128)(2,1)S(1)} %fusion.32), channel_id=1, source_target_pairs={{0,8},{2,10},{4,12},{6,14},{8,0},{10,2},{12,4},{14,6},{1,9},{3,11}... | collective-permute-start | bytes 98312 | tf_op jit(solution)/shard_map/ppermute | solution.py:19
  79.5 4.9 %collective-permute-start.37 = (bf16[16,1024]{1,0:T(8,128)(2,1)S(1)}, bf16[16,1024]{1,0:T(8,128)(2,1)S(1)}, u32[]{:S(2)}, u32[]{:S(2)}) collective-permute-start(bf16[16,1024]{1,0:T(8,128)(2,1)S(1)} %fusion.33), channel_id=1, source_target_pairs={{0,8},{2,10},{4,12},{6,14},{8,0},{10,2},{12,4},{14,6},{1,9},{3,11}... | collective-permute-start | bytes 98312 | tf_op jit(solution)/shard_map/ppermute | solution.py:19

commit v28 on v25

--- a/solution.py
+++ b/solution.py
@@ -9,6 +9,7 @@
 from jax.sharding import PartitionSpec as P
 
 CHUNKS = 4
+LINK_TYPES = (jnp.bfloat16, jnp.float32, jnp.bfloat16)
 TILE = 512
 KERNEL_VMEM = 50 * 2**20
 
@@ -46,13 +47,13 @@
     rows, cols = value.shape[0] >> len(order), value.shape[1]
     total = value.reshape([2] * len(order) + [rows, cols])
     left = sorted(order, reverse=True)
-    for bit in order:
+    for step, bit in enumerate(order):
         dim = left.index(bit)
         left.remove(bit)
         low = lax.index_in_dim(total, 0, dim, keepdims=False)
         high = lax.index_in_dim(total, 1, dim, keepdims=False)
         upper = bit_of(axis, bit) == 1
-        send = jnp.where(upper, low, high).astype(jnp.bfloat16)
+        send = jnp.where(upper, low, high).astype(LINK_TYPES[min(step, 2)])
         landed = swap(send, axis, 1 << bit)
         total = jnp.where(upper, high, low) + landed.astype(jnp.float32)
     return total
@@ -63,11 +64,11 @@
 
 
 def sum_and_share(value, axis, order, scale):
-    for bit in order[:-1]:
+    for step, bit in enumerate(order[:-1]):
         upper = bit_of(axis, bit) == 1
         half = value.shape[1] // 2
         low, high = value[:, :half], value[:, half:]
-        send = jnp.where(upper, low, high).astype(jnp.bfloat16)
+        send = jnp.where(upper, low, high).astype(LINK_TYPES[min(step, 2)])
         landed = swap(send, axis, 1 << bit)
         value = jnp.where(upper, high, low) + landed.astype(jnp.float32)
     landed = swap(value.astype(jnp.bfloat16), axis, 1 << order[-1])

time: 81.8 us -> 85 us (1.039)
  starting transfers between devices: 44.5 us -> 46.8 us
  waiting for transfers between devices: 22.3 us -> 23.3 us
    ppermute x34, starting transfers between devices: 39.4 us -> 41.7 us  [swap(): return lax.ppermute(value, axis, [(i, i ^ distance) for i in range(size)])]
    ppermute x4, waiting for transfers between devices: 2.67 us -> 3.74 us  [row_sum(): terms.append(lax.ppermute(value, ('row', 'col'), pairs))]
  transfers between devices with their start and end apart: 38 -> 38, of which waited for: 19 -> 21; matrix products, arithmetic and copies ran while one was open for 3% -> 3% of each run, Pallas kernels for 2% -> 2%
where the time goes in v28:
time: 85 us; the launch traced here: 84.8 us
  starting transfers between devices  46.8 us (55%)
  waiting for transfers between devices  23.3 us (27%)
  Pallas kernels  8.67 us (10%)
  other arithmetic  2.1 us (2%)
  matrix products  1.77 us (2%)
  between operations  1.1 us (1%)
  local copies, waits for them, and re-layouts  1.05 us (1%)
    ppermute x34, starting transfers between devices, swap(): return lax.ppermute(value, axis, [(i, i ^ distance) for i in range(size)])  41.7 us
    ppermute x34, waiting for transfers between devices, swap(): return lax.ppermute(value, axis, [(i, i ^ distance) for i in range(size)])  19.6 us
    ppermute x4, starting transfers between devices, row_sum(): terms.append(lax.ppermute(value, ('row', 'col'), pairs))  5.1 us
    pallas_call x1, Pallas kernels, make_basis(): pl.pallas_call(functools.partial(basis_kernel, root_rows), out_shape=[jax...  4.1 us
    pallas_call x2, Pallas kernels, first_product(): pl.pallas_call(functools.partial(sketch_kernel, begin), out_shape=[jax.Sh...  4.07 us
    ppermute x4, waiting for transfers between devices, row_sum(): terms.append(lax.ppermute(value, ('row', 'col'), pairs))  3.74 us
    dot_general x4, matrix products, per_device(): lax.dot_general(activations[:, span], shared, (((1,), (1,)), ((), ())), p...  1.77 us
  transfers between devices with their start and end apart: 38, of which 21 were waited for; matrix products, arithmetic and copies ran while one was open for 3% of the time, Pallas kernels for 2%

profile of v28, /device:TPU:0, one launch (start us, length us, event | category | flops | bytes accessed | tf_op | source)
XLA Modules:
  0.0 84.8 jit_solution(6884572930004887046)
XLA Ops:
  0.7 0.9 %copy-done = bf16[512,128]{1,0:T(8,128)(2,1)S(1)} copy-done((bf16[512,128]{1,0:T(8,128)(2,1)S(1)}, bf16[512,128]{1,0:T(8,128)(2,1)}, u32[]{:S(2)}) %copy-start) | copy-done | bytes 131096
  1.6 2.1 %first_product.3 = (f32[128,1024]{1,0:T(8,128)S(1)}, f32[128,1024]{1,0:T(8,128)S(1)}) custom-call(bf16[512,128]{1,0:T(8,128)(2,1)S(1)} %copy-done, bf16[512,4096]{1,0:T(8,128)(2,1)} %slab_ref.5), custom_call_target="tpu_custom_call" | custom-call | flops 268435456 | bytes 2097152 | tf_op jit(solution)/shard_map/first_product/pallas_call | solution.py:118
  3.6 3.1 %collective-permute-start.15 = (bf16[128,512]{1,0:T(8,128)(2,1)S(1)}, bf16[128,512]{1,0:T(8,128)(2,1)S(1)}, u32[]{:S(2)}, u32[]{:S(2)}) collective-permute-start(bf16[128,512]{1,0:T(8,128)(2,1)S(1)} %select_convert_fusion.4), channel_id=1, source_target_pairs={{0,4},{2,6},{4,0},{6,2},{8,12},{10,14},{12,8},{14,10},{1,5},{3,7},... | collective-permute-start | bytes 393224 | tf_op jit(solution)/shard_map/ppermute | solution.py:19
  6.8 1.6 %collective-permute-start.10 = (bf16[128,512]{1,0:T(8,128)(2,1)S(1)}, bf16[128,512]{1,0:T(8,128)(2,1)S(1)}, u32[]{:S(2)}, u32[]{:S(2)}) collective-permute-start(bf16[128,512]{1,0:T(8,128)(2,1)S(1)} %select_convert_fusion.5), channel_id=1, source_target_pairs={{0,2},{2,0},{4,6},{6,4},{8,10},{10,8},{12,14},{14,12},{1,3},{3,1},... | collective-permute-start | bytes 393224 | tf_op jit(solution)/shard_map/ppermute | solution.py:19
  8.3 2.0 %first_product.2 = (f32[128,1024]{1,0:T(8,128)S(1)}, f32[128,1024]{1,0:T(8,128)S(1)}) custom-call(bf16[512,128]{1,0:T(8,128)(2,1)S(1)} %copy-done.1, bf16[512,4096]{1,0:T(8,128)(2,1)} %slab_ref.5), custom_call_target="tpu_custom_call" | custom-call | flops 268435456 | bytes 2097152 | tf_op jit(solution)/shard_map/first_product/pallas_call | solution.py:118
  11.2 2.0 %collective-permute-start.16 = (f32[128,256]{1,0:T(8,128)S(1)}, f32[128,256]{1,0:T(8,128)S(1)}, u32[]{:S(2)}, u32[]{:S(2)}) collective-permute-start(f32[128,256]{1,0:T(8,128)S(1)} %slice_select_fusion), channel_id=1, source_target_pairs={{0,2},{2,0},{4,6},{6,4},{8,10},{10,8},{12,14},{14,12},{1,3},{3,1},... | collective-permute-start | bytes 393224 | tf_op jit(solution)/shard_map/ppermute | solution.py:19
  13.3 1.6 %collective-permute-start.11 = (f32[128,256]{1,0:T(8,128)S(1)}, f32[128,256]{1,0:T(8,128)S(1)}, u32[]{:S(2)}, u32[]{:S(2)}) collective-permute-start(f32[128,256]{1,0:T(8,128)S(1)} %slice_select_fusion.1), channel_id=1, source_target_pairs={{0,4},{2,6},{4,0},{6,2},{8,12},{10,14},{12,8},{14,10},{1,5},{3,7},... | collective-permute-start | bytes 393224 | tf_op jit(solution)/shard_map/ppermute | solution.py:19
  14.9 1.6 %collective-permute-done.5 = bf16[128,512]{1,0:T(8,128)(2,1)S(1)} collective-permute-done((bf16[128,512]{1,0:T(8,128)(2,1)S(1)}, bf16[128,512]{1,0:T(8,128)(2,1)S(1)}, u32[]{:S(2)}, u32[]{:S(2)}) %collective-permute-start.5) | collective-permute-done | bytes 131104 | tf_op jit(solution)/shard_map/ppermute | solution.py:19
  16.6 0.8 collective-permute-start.6
  17.4 1.8 %collective-permute-start.1 = (f32[128,256]{1,0:T(8,128)S(1)}, f32[128,256]{1,0:T(8,128)S(1)}, u32[]{:S(2)}, u32[]{:S(2)}) collective-permute-start(f32[128,256]{1,0:T(8,128)S(1)} %slice_select_fusion.3), channel_id=1, source_target_pairs={{0,4},{2,6},{4,0},{6,2},{8,12},{10,14},{12,8},{14,10},{1,5},{3,7},... | collective-permute-start | bytes 393224 | tf_op jit(solution)/shard_map/ppermute | solution.py:19
  19.6 2.7 %collective-permute-start.17 = (bf16[128,256]{1,0:T(8,128)(2,1)S(1)}, bf16[128,256]{1,0:T(8,128)(2,1)S(1)}, u32[]{:S(2)}, u32[]{:S(2)}) collective-permute-start(bf16[128,256]{1,0:T(8,128)(2,1)S(1)} %get-tuple-element.30), channel_id=1, source_target_pairs={{0,8},{2,10},{4,12},{6,14},{8,0},{10,2},{12,4},{14,6},{1,9},{3,11}... | collective-permute-start | bytes 196616 | tf_op jit(solution)/shard_map/ppermute | solution.py:19
  22.8 2.7 %collective-permute-start.7 = (bf16[128,256]{1,0:T(8,128)(2,1)S(1)}, bf16[128,256]{1,0:T(8,128)(2,1)S(1)}, u32[]{:S(2)}, u32[]{:S(2)}) collective-permute-start(bf16[128,256]{1,0:T(8,128)(2,1)S(1)} %get-tuple-element.26), channel_id=1, source_target_pairs={{0,8},{2,10},{4,12},{6,14},{8,0},{10,2},{12,4},{14,6},{1,9},{3,11}... | collective-permute-start | bytes 196616 | tf_op jit(solution)/shard_map/ppermute | solution.py:19
  25.4 0.7 collective-permute-start.2
  26.1 1.3 %collective-permute-done.17 = bf16[128,256]{1,0:T(8,128)(2,1)S(1)} collective-permute-done((bf16[128,256]{1,0:T(8,128)(2,1)S(1)}, bf16[128,256]{1,0:T(8,128)(2,1)S(1)}, u32[]{:S(2)}, u32[]{:S(2)}) %collective-permute-start.17) | collective-permute-done | bytes 65568 | tf_op jit(solution)/shard_map/ppermute | solution.py:19
  27.5 0.9 %collective-permute-start.18 = (bf16[128,256]{1,0:T(8,128)(2,1)S(1)}, bf16[128,256]{1,0:T(8,128)(2,1)S(1)}, u32[]{:S(2)}, u32[]{:S(2)}) collective-permute-start(bf16[128,256]{1,0:T(8,128)(2,1)S(1)} %multiply_convert_fusion), channel_id=1, source_target_pairs={{0,2},{2,0},{4,6},{6,4},{8,10},{10,8},{12,14},{14,12},{1,3},{3,1},... | collective-permute-start | bytes 196616 | tf_op jit(solution)/shard_map/ppermute | solution.py:19
  28.4 1.7 %collective-permute-done.12 = bf16[128,256]{1,0:T(8,128)(2,1)S(1)} collective-permute-done((bf16[128,256]{1,0:T(8,128)(2,1)S(1)}, bf16[128,256]{1,0:T(8,128)(2,1)S(1)}, u32[]{:S(2)}, u32[]{:S(2)}) %collective-permute-start.12) | collective-permute-done | bytes 65568 | tf_op jit(solution)/shard_map/ppermute | solution.py:19
  30.8 0.9 %collective-permute-start.8 = (bf16[128,256]{1,0:T(8,128)(2,1)S(1)}, bf16[128,256]{1,0:T(8,128)(2,1)S(1)}, u32[]{:S(2)}, u32[]{:S(2)}) collective-permute-start(bf16[128,256]{1,0:T(8,128)(2,1)S(1)} %multiply_convert_fusion.2), channel_id=1, source_target_pairs={{0,2},{2,0},{4,6},{6,4},{8,10},{10,8},{12,14},{14,12},{1,3},{3,1},... | collective-permute-start | bytes 196616 | tf_op jit(solution)/shard_map/ppermute | solution.py:19
  32.2 1.0 %collective-permute-start.3 = (bf16[128,256]{1,0:T(8,128)(2,1)S(1)}, bf16[128,256]{1,0:T(8,128)(2,1)S(1)}, u32[]{:S(2)}, u32[]{:S(2)}) collective-permute-start(bf16[128,256]{1,0:T(8,128)(2,1)S(1)} %multiply_convert_fusion.3), channel_id=1, source_target_pairs={{0,4},{2,6},{4,0},{6,2},{8,12},{10,14},{12,8},{14,10},{1,5},{3,7},... | collective-permute-start | bytes 196616 | tf_op jit(solution)/shard_map/ppermute | solution.py:19
  33.2 1.2 %collective-permute-start.19 = (bf16[128,512]{1,0:T(8,128)(2,1)S(1)}, bf16[128,512]{1,0:T(8,128)(2,1)S(1)}, u32[]{:S(2)}, u32[]{:S(2)}) collective-permute-start(bf16[128,512]{1,0:T(8,128)(2,1)S(1)} %pad_maximum_fusion.4), channel_id=1, source_target_pairs={{0,4},{2,6},{4,0},{6,2},{8,12},{10,14},{12,8},{14,10},{1,5},{3,7},... | collective-permute-start | bytes 393224 | tf_op jit(solution)/shard_map/ppermute | solution.py:19
  34.4 0.7 collective-permute-done.13
  35.2 0.9 %collective-permute-start.14 = (bf16[128,512]{1,0:T(8,128)(2,1)S(1)}, bf16[128,512]{1,0:T(8,128)(2,1)S(1)}, u32[]{:S(2)}, u32[]{:S(2)}) collective-permute-start(bf16[128,512]{1,0:T(8,128)(2,1)S(1)} %pad_maximum_fusion.3), channel_id=1, source_target_pairs={{0,2},{2,0},{4,6},{6,4},{8,10},{10,8},{12,14},{14,12},{1,3},{3,1},... | collective-permute-start | bytes 393224 | tf_op jit(solution)/shard_map/ppermute | solution.py:19
  36.1 1.1 %collective-permute-start.9 = (bf16[128,512]{1,0:T(8,128)(2,1)S(1)}, bf16[128,512]{1,0:T(8,128)(2,1)S(1)}, u32[]{:S(2)}, u32[]{:S(2)}) collective-permute-start(bf16[128,512]{1,0:T(8,128)(2,1)S(1)} %pad_maximum_fusion.2), channel_id=1, source_target_pairs={{0,4},{2,6},{4,0},{6,2},{8,12},{10,14},{12,8},{14,10},{1,5},{3,7},... | collective-permute-start | bytes 393224 | tf_op jit(solution)/shard_map/ppermute | solution.py:19
  37.3 0.9 %collective-permute-start.4 = (bf16[128,512]{1,0:T(8,128)(2,1)S(1)}, bf16[128,512]{1,0:T(8,128)(2,1)S(1)}, u32[]{:S(2)}, u32[]{:S(2)}) collective-permute-start(bf16[128,512]{1,0:T(8,128)(2,1)S(1)} %pad_maximum_fusion.1), channel_id=1, source_target_pairs={{0,2},{2,0},{4,6},{6,4},{8,10},{10,8},{12,14},{14,12},{1,3},{3,1},... | collective-permute-start | bytes 393224 | tf_op jit(solution)/shard_map/ppermute | solution.py:19
  38.2 0.8 collective-permute-done.19
  39.5 0.7 collective-permute-done.14
  41.6 0.8 collective-permute-done.4
  43.0 1.5 %collective-permute-done.20.other_ref = f32[512,128]{1,0:T(8,128)S(1)} collective-permute-done((f32[512,128]{1,0:T(8,128)S(1)}, f32[512,128]{1,0:T(8,128)S(1)}, u32[]{:S(2)}, u32[]{:S(2)}) %collective-permute-start.20) | collective-permute-done | bytes 262176 | tf_op jit(solution)/shard_map/ppermute | solution.py:19
  45.0 3.4 %collective-permute-start.24 = (f32[72,128]{1,0:T(8,128)S(1)}, f32[72,128]{1,0:T(8,128)S(1)}, u32[]{:S(2)}, u32[]{:S(2)}) collective-permute-start(f32[72,128]{1,0:T(8,128)S(1)} %get-tuple-element.17), channel_id=1, source_target_pairs={{0,10},{1,15},{2,8},{3,13},{4,14},{5,11},{6,12},{7,9},{8,2},{9,7},... | collective-permute-start | bytes 110600 | tf_op jit(solution)/shard_map/ppermute | solution.py:37
  48.4 1.1 %collective-permute-start.22 = (f32[72,128]{1,0:T(8,128)S(1)}, f32[72,128]{1,0:T(8,128)S(1)}, u32[]{:S(2)}, u32[]{:S(2)}) collective-permute-start(f32[72,128]{1,0:T(8,128)S(1)} %get-tuple-element.17), channel_id=1, source_target_pairs={{0,2},{1,7},{2,0},{3,5},{4,6},{5,3},{6,4},{7,1},{8,10},{9,15},{10,... | collective-permute-start | bytes 110600 | tf_op jit(solution)/shard_map/ppermute | solution.py:37
  50.1 1.7 %collective-permute-done.24 = f32[72,128]{1,0:T(8,128)S(1)} collective-permute-done((f32[72,128]{1,0:T(8,128)S(1)}, f32[72,128]{1,0:T(8,128)S(1)}, u32[]{:S(2)}, u32[]{:S(2)}) %collective-permute-start.24) | collective-permute-done | bytes 36896 | tf_op jit(solution)/shard_map/ppermute | solution.py:37
  51.8 2.0 %collective-permute-done.23 = f32[72,128]{1,0:T(8,128)S(1)} collective-permute-done((f32[72,128]{1,0:T(8,128)S(1)}, f32[72,128]{1,0:T(8,128)S(1)}, u32[]{:S(2)}, u32[]{:S(2)}) %collective-permute-start.23) | collective-permute-done | bytes 36896 | tf_op jit(solution)/shard_map/ppermute | solution.py:37
  54.1 1.0 %collective-permute-done.25 = f32[72,128]{1,0:T(8,128)S(1)} collective-permute-done((f32[72,128]{1,0:T(8,128)S(1)}, f32[72,128]{1,0:T(8,128)S(1)}, u32[]{:S(2)}, u32[]{:S(2)}) %collective-permute-start.25) | collective-permute-done | bytes 36896 | tf_op jit(solution)/shard_map/ppermute | solution.py:19
  55.2 4.1 %make_basis.1 = (f32[512,128]{1,0:T(8,128)}, f32[128,1024]{1,0:T(8,128)S(1)}, f32[128,1024]{1,0:T(8,128)S(1)}, f32[128,1024]{1,0:T(8,128)S(1)}, f32[128,1024]{1,0:T(8,128)S(1)}) custom-call(f32[72,128]{1,0:T(8,128)S(1)} %add.116.gram_ref, f32[128,512]{1,0:T(8,128)S(1)} %get-tuple-element.18.sketch_ref, bf16[512,4096]{1,0:T(8,128)(2,1)} %slab_ref.5), custom_call_target="tpu_custom_call" | custom-call | tf_op jit(solution)/shard_map/make_basis/pallas_call | solution.py:280
  59.3 0.7 collective-permute-start.26
  60.1 1.8 %collective-permute-start.29 = (bf16[2,2,16,1024]{3,2,0,1:T(8,128)(2,1)S(1)}, bf16[2,2,16,1024]{3,2,0,1:T(8,128)(2,1)S(1)}, u32[]{:S(2)}, u32[]{:S(2)}) collective-permute-start(bf16[2,2,16,1024]{3,2,0,1:T(8,128)(2,1)S(1)} %fusion.23), channel_id=1, source_target_pairs={{0,4},{2,6},{4,0},{6,2},{8,12},{10,14},{12,8},{14,10},{1,5},{3,7},... | collective-permute-start | bytes 393224 | tf_op jit(solution)/shard_map/ppermute | solution.py:19
  62.0 1.3 %collective-permute-start.32 = (bf16[2,2,16,1024]{3,2,0,1:T(8,128)(2,1)S(1)}, bf16[2,2,16,1024]{3,2,0,1:T(8,128)(2,1)S(1)}, u32[]{:S(2)}, u32[]{:S(2)}) collective-permute-start(bf16[2,2,16,1024]{3,2,0,1:T(8,128)(2,1)S(1)} %fusion.24), channel_id=1, source_target_pairs={{0,2},{2,0},{4,6},{6,4},{8,10},{10,8},{12,14},{14,12},{1,3},{3,1},... | collective-permute-start | bytes 393224 | tf_op jit(solution)/shard_map/ppermute | solution.py:19
  63.9 1.6 %collective-permute-done.26 = bf16[2,2,16,1024]{3,2,0,1:T(8,128)(2,1)S(1)} collective-permute-done((bf16[2,2,16,1024]{3,2,0,1:T(8,128)(2,1)S(1)}, bf16[2,2,16,1024]{3,2,0,1:T(8,128)(2,1)S(1)}, u32[]{:S(2)}, u32[]{:S(2)}) %collective-permute-start.26) | collective-permute-done | bytes 131104 | tf_op jit(solution)/shard_map/ppermute | solution.py:19
  65.6 1.9 %collective-permute-start.27 = (f32[2,16,1024]{2,1,0:T(8,128)S(1)}, f32[2,16,1024]{2,1,0:T(8,128)S(1)}, u32[]{:S(2)}, u32[]{:S(2)}) collective-permute-start(f32[2,16,1024]{2,1,0:T(8,128)S(1)} %select_bitcast_fusion.3), channel_id=1, source_target_pairs={{0,4},{2,6},{4,0},{6,2},{8,12},{10,14},{12,8},{14,10},{1,5},{3,7},... | collective-permute-start | bytes 393224 | tf_op jit(solution)/shard_map/ppermute | solution.py:19
  67.5 0.8 collective-permute-start.30
  68.4 1.4 %collective-permute-start.33 = (f32[2,16,1024]{2,1,0:T(8,128)S(1)}, f32[2,16,1024]{2,1,0:T(8,128)S(1)}, u32[]{:S(2)}, u32[]{:S(2)}) collective-permute-start(f32[2,16,1024]{2,1,0:T(8,128)S(1)} %select_bitcast_fusion.1), channel_id=1, source_target_pairs={{0,4},{2,6},{4,0},{6,2},{8,12},{10,14},{12,8},{14,10},{1,5},{3,7},... | collective-permute-start | bytes 393224 | tf_op jit(solution)/shard_map/ppermute | solution.py:19
  69.9 0.9 %collective-permute-start.36 = (f32[2,16,1024]{2,1,0:T(8,128)S(1)}, f32[2,16,1024]{2,1,0:T(8,128)S(1)}, u32[]{:S(2)}, u32[]{:S(2)}) collective-permute-start(f32[2,16,1024]{2,1,0:T(8,128)S(1)} %select_bitcast_fusion), channel_id=1, source_target_pairs={{0,2},{2,0},{4,6},{6,4},{8,10},{10,8},{12,14},{14,12},{1,3},{3,1},... | collective-permute-start | bytes 393224 | tf_op jit(solution)/shard_map/ppermute | solution.py:19
  70.8 1.6 %collective-permute-done.27 = f32[2,16,1024]{2,1,0:T(8,128)S(1)} collective-permute-done((f32[2,16,1024]{2,1,0:T(8,128)S(1)}, f32[2,16,1024]{2,1,0:T(8,128)S(1)}, u32[]{:S(2)}, u32[]{:S(2)}) %collective-permute-start.27) | collective-permute-done | bytes 131104 | tf_op jit(solution)/shard_map/ppermute | solution.py:19
  72.4 3.3 %collective-permute-start.28 = (bf16[16,1024]{1,0:T(8,128)(2,1)S(1)}, bf16[16,1024]{1,0:T(8,128)(2,1)S(1)}, u32[]{:S(2)}, u32[]{:S(2)}) collective-permute-start(bf16[16,1024]{1,0:T(8,128)(2,1)S(1)} %fusion.30), channel_id=1, source_target_pairs={{0,8},{2,10},{4,12},{6,14},{8,0},{10,2},{12,4},{14,6},{1,9},{3,11}... | collective-permute-start | bytes 98312 | tf_op jit(solution)/shard_map/ppermute | solution.py:19
  76.4 2.5 %collective-permute-start.34 = (bf16[16,1024]{1,0:T(8,128)(2,1)S(1)}, bf16[16,1024]{1,0:T(8,128)(2,1)S(1)}, u32[]{:S(2)}, u32[]{:S(2)}) collective-permute-start(bf16[16,1024]{1,0:T(8,128)(2,1)S(1)} %fusion.32), channel_id=1, source_target_pairs={{0,8},{2,10},{4,12},{6,14},{8,0},{10,2},{12,4},{14,6},{1,9},{3,11}... | collective-permute-start | bytes 98312 | tf_op jit(solution)/shard_map/ppermute | solution.py:19
  79.5 1.6 %collective-permute-done.31 = bf16[16,1024]{1,0:T(8,128)(2,1)S(1)} collective-permute-done((bf16[16,1024]{1,0:T(8,128)(2,1)S(1)}, bf16[16,1024]{1,0:T(8,128)(2,1)S(1)}, u32[]{:S(2)}, u32[]{:S(2)}) %collective-permute-start.31) | collective-permute-done | bytes 32800 | tf_op jit(solution)/shard_map/ppermute | solution.py:19
  81.2 0.7 collective-permute-done.34
  81.9 2.2 %collective-permute-done.37 = bf16[16,1024]{1,0:T(8,128)(2,1)S(1)} collective-permute-done((bf16[16,1024]{1,0:T(8,128)(2,1)S(1)}, bf16[16,1024]{1,0:T(8,128)(2,1)S(1)}, u32[]{:S(2)}, u32[]{:S(2)}) %collective-permute-start.37) | collective-permute-done | bytes 32800 | tf_op jit(solution)/shard_map/ppermute | solution.py:19
  84.1 0.7 pad_maximum_fusion
  (105 shorter events, 9.7 us)
Async XLA Ops:
  0.6 0.9 %copy-start = (bf16[512,128]{1,0:T(8,128)(2,1)S(1)}, bf16[512,128]{1,0:T(8,128)(2,1)}, u32[]{:S(2)}) copy-start(bf16[512,128]{1,0:T(8,128)(2,1)} %start_ref.3) | copy-start | bytes 393220
  1.6 6.8 %copy-start.1 = (bf16[512,128]{1,0:T(8,128)(2,1)S(1)}, bf16[512,128]{1,0:T(8,128)(2,1)}, u32[]{:S(2)}) copy-start(bf16[512,128]{1,0:T(8,128)(2,1)} %start_ref.3) | copy-start | bytes 393220
  3.6 7.5 %collective-permute-start.15 = (bf16[128,512]{1,0:T(8,128)(2,1)S(1)}, bf16[128,512]{1,0:T(8,128)(2,1)S(1)}, u32[]{:S(2)}, u32[]{:S(2)}) collective-permute-start(bf16[128,512]{1,0:T(8,128)(2,1)S(1)} %select_convert_fusion.4), channel_id=1, source_target_pairs={{0,4},{2,6},{4,0},{6,2},{8,12},{10,14},{12,8},{14,10},{1,5},{3,7},... | collective-permute-start | bytes 393224 | tf_op jit(solution)/shard_map/ppermute | solution.py:19
  6.8 6.4 %collective-permute-start.10 = (bf16[128,512]{1,0:T(8,128)(2,1)S(1)}, bf16[128,512]{1,0:T(8,128)(2,1)S(1)}, u32[]{:S(2)}, u32[]{:S(2)}) collective-permute-start(bf16[128,512]{1,0:T(8,128)(2,1)S(1)} %select_convert_fusion.5), channel_id=1, source_target_pairs={{0,2},{2,0},{4,6},{6,4},{8,10},{10,8},{12,14},{14,12},{1,3},{3,1},... | collective-permute-start | bytes 393224 | tf_op jit(solution)/shard_map/ppermute | solution.py:19
  10.4 6.1 %collective-permute-start.5 = (bf16[128,512]{1,0:T(8,128)(2,1)S(1)}, bf16[128,512]{1,0:T(8,128)(2,1)S(1)}, u32[]{:S(2)}, u32[]{:S(2)}) collective-permute-start(bf16[128,512]{1,0:T(8,128)(2,1)S(1)} %select_convert_fusion.6), channel_id=1, source_target_pairs={{0,4},{2,6},{4,0},{6,2},{8,12},{10,14},{12,8},{14,10},{1,5},{3,7},... | collective-permute-start | bytes 393224 | tf_op jit(solution)/shard_map/ppermute | solution.py:19
  10.9 6.4 %collective-permute-start = (bf16[128,512]{1,0:T(8,128)(2,1)S(1)}, bf16[128,512]{1,0:T(8,128)(2,1)S(1)}, u32[]{:S(2)}, u32[]{:S(2)}) collective-permute-start(bf16[128,512]{1,0:T(8,128)(2,1)S(1)} %select_convert_fusion.7), channel_id=1, source_target_pairs={{0,2},{2,0},{4,6},{6,4},{8,10},{10,8},{12,14},{14,12},{1,3},{3,1},... | collective-permute-start | bytes 393224 | tf_op jit(solution)/shard_map/ppermute | solution.py:19
  11.2 8.4 %collective-permute-start.16 = (f32[128,256]{1,0:T(8,128)S(1)}, f32[128,256]{1,0:T(8,128)S(1)}, u32[]{:S(2)}, u32[]{:S(2)}) collective-permute-start(f32[128,256]{1,0:T(8,128)S(1)} %slice_select_fusion), channel_id=1, source_target_pairs={{0,2},{2,0},{4,6},{6,4},{8,10},{10,8},{12,14},{14,12},{1,3},{3,1},... | collective-permute-start | bytes 393224 | tf_op jit(solution)/shard_map/ppermute | solution.py:19
  13.2 25.8 %copy-start.2 = (bf16[512,4096]{1,0:T(8,128)(2,1)S(1)}, bf16[512,4096]{1,0:T(8,128)(2,1)}, u32[]{:S(2)}) copy-start(bf16[512,4096]{1,0:T(8,128)(2,1)} %slab_ref.5) | copy-start | bytes 12582916
  13.3 9.0 %collective-permute-start.11 = (f32[128,256]{1,0:T(8,128)S(1)}, f32[128,256]{1,0:T(8,128)S(1)}, u32[]{:S(2)}, u32[]{:S(2)}) collective-permute-start(f32[128,256]{1,0:T(8,128)S(1)} %slice_select_fusion.1), channel_id=1, source_target_pairs={{0,4},{2,6},{4,0},{6,2},{8,12},{10,14},{12,8},{14,10},{1,5},{3,7},... | collective-permute-start | bytes 393224 | tf_op jit(solution)/shard_map/ppermute | solution.py:19
  16.6 6.2 %collective-permute-start.6 = (f32[128,256]{1,0:T(8,128)S(1)}, f32[128,256]{1,0:T(8,128)S(1)}, u32[]{:S(2)}, u32[]{:S(2)}) collective-permute-start(f32[128,256]{1,0:T(8,128)S(1)} %slice_select_fusion.2), channel_id=1, source_target_pairs={{0,2},{2,0},{4,6},{6,4},{8,10},{10,8},{12,14},{14,12},{1,3},{3,1},... | collective-permute-start | bytes 393224 | tf_op jit(solution)/shard_map/ppermute | solution.py:19
  17.4 8.0 %collective-permute-start.1 = (f32[128,256]{1,0:T(8,128)S(1)}, f32[128,256]{1,0:T(8,128)S(1)}, u32[]{:S(2)}, u32[]{:S(2)}) collective-permute-start(f32[128,256]{1,0:T(8,128)S(1)} %slice_select_fusion.3), channel_id=1, source_target_pairs={{0,4},{2,6},{4,0},{6,2},{8,12},{10,14},{12,8},{14,10},{1,5},{3,7},... | collective-permute-start | bytes 393224 | tf_op jit(solution)/shard_map/ppermute | solution.py:19
  19.6 7.8 %collective-permute-start.17 = (bf16[128,256]{1,0:T(8,128)(2,1)S(1)}, bf16[128,256]{1,0:T(8,128)(2,1)S(1)}, u32[]{:S(2)}, u32[]{:S(2)}) collective-permute-start(bf16[128,256]{1,0:T(8,128)(2,1)S(1)} %get-tuple-element.30), channel_id=1, source_target_pairs={{0,8},{2,10},{4,12},{6,14},{8,0},{10,2},{12,4},{14,6},{1,9},{3,11}... | collective-permute-start | bytes 196616 | tf_op jit(solution)/shard_map/ppermute | solution.py:19
  22.3 7.8 %collective-permute-start.12 = (bf16[128,256]{1,0:T(8,128)(2,1)S(1)}, bf16[128,256]{1,0:T(8,128)(2,1)S(1)}, u32[]{:S(2)}, u32[]{:S(2)}) collective-permute-start(bf16[128,256]{1,0:T(8,128)(2,1)S(1)} %get-tuple-element.28), channel_id=1, source_target_pairs={{0,8},{2,10},{4,12},{6,14},{8,0},{10,2},{12,4},{14,6},{1,9},{3,11}... | collective-permute-start | bytes 196616 | tf_op jit(solution)/shard_map/ppermute | solution.py:19
  22.8 8.0 %collective-permute-start.7 = (bf16[128,256]{1,0:T(8,128)(2,1)S(1)}, bf16[128,256]{1,0:T(8,128)(2,1)S(1)}, u32[]{:S(2)}, u32[]{:S(2)}) collective-permute-start(bf16[128,256]{1,0:T(8,128)(2,1)S(1)} %get-tuple-element.26), channel_id=1, source_target_pairs={{0,8},{2,10},{4,12},{6,14},{8,0},{10,2},{12,4},{14,6},{1,9},{3,11}... | collective-permute-start | bytes 196616 | tf_op jit(solution)/shard_map/ppermute | solution.py:19
  25.4 6.7 %collective-permute-start.2 = (bf16[128,256]{1,0:T(8,128)(2,1)S(1)}, bf16[128,256]{1,0:T(8,128)(2,1)S(1)}, u32[]{:S(2)}, u32[]{:S(2)}) collective-permute-start(bf16[128,256]{1,0:T(8,128)(2,1)S(1)} %get-tuple-element.24), channel_id=1, source_target_pairs={{0,8},{2,10},{4,12},{6,14},{8,0},{10,2},{12,4},{14,6},{1,9},{3,11}... | collective-permute-start | bytes 196616 | tf_op jit(solution)/shard_map/ppermute | solution.py:19
  27.5 5.7 %collective-permute-start.18 = (bf16[128,256]{1,0:T(8,128)(2,1)S(1)}, bf16[128,256]{1,0:T(8,128)(2,1)S(1)}, u32[]{:S(2)}, u32[]{:S(2)}) collective-permute-start(bf16[128,256]{1,0:T(8,128)(2,1)S(1)} %multiply_convert_fusion), channel_id=1, source_target_pairs={{0,2},{2,0},{4,6},{6,4},{8,10},{10,8},{12,14},{14,12},{1,3},{3,1},... | collective-permute-start | bytes 196616 | tf_op jit(solution)/shard_map/ppermute | solution.py:19
  30.1 5.0 %collective-permute-start.13 = (bf16[128,256]{1,0:T(8,128)(2,1)S(1)}, bf16[128,256]{1,0:T(8,128)(2,1)S(1)}, u32[]{:S(2)}, u32[]{:S(2)}) collective-permute-start(bf16[128,256]{1,0:T(8,128)(2,1)S(1)} %multiply_convert_fusion.1), channel_id=1, source_target_pairs={{0,4},{2,6},{4,0},{6,2},{8,12},{10,14},{12,8},{14,10},{1,5},{3,7},... | collective-permute-start | bytes 196616 | tf_op jit(solution)/shard_map/ppermute | solution.py:19
  30.8 5.2 %collective-permute-start.8 = (bf16[128,256]{1,0:T(8,128)(2,1)S(1)}, bf16[128,256]{1,0:T(8,128)(2,1)S(1)}, u32[]{:S(2)}, u32[]{:S(2)}) collective-permute-start(bf16[128,256]{1,0:T(8,128)(2,1)S(1)} %multiply_convert_fusion.2), channel_id=1, source_target_pairs={{0,2},{2,0},{4,6},{6,4},{8,10},{10,8},{12,14},{14,12},{1,3},{3,1},... | collective-permute-start | bytes 196616 | tf_op jit(solution)/shard_map/ppermute | solution.py:19
  32.2 5.1 %collective-permute-start.3 = (bf16[128,256]{1,0:T(8,128)(2,1)S(1)}, bf16[128,256]{1,0:T(8,128)(2,1)S(1)}, u32[]{:S(2)}, u32[]{:S(2)}) collective-permute-start(bf16[128,256]{1,0:T(8,128)(2,1)S(1)} %multiply_convert_fusion.3), channel_id=1, source_target_pairs={{0,4},{2,6},{4,0},{6,2},{8,12},{10,14},{12,8},{14,10},{1,5},{3,7},... | collective-permute-start | bytes 196616 | tf_op jit(solution)/shard_map/ppermute | solution.py:19
  33.2 5.8 %collective-permute-start.19 = (bf16[128,512]{1,0:T(8,128)(2,1)S(1)}, bf16[128,512]{1,0:T(8,128)(2,1)S(1)}, u32[]{:S(2)}, u32[]{:S(2)}) collective-permute-start(bf16[128,512]{1,0:T(8,128)(2,1)S(1)} %pad_maximum_fusion.4), channel_id=1, source_target_pairs={{0,4},{2,6},{4,0},{6,2},{8,12},{10,14},{12,8},{14,10},{1,5},{3,7},... | collective-permute-start | bytes 393224 | tf_op jit(solution)/shard_map/ppermute | solution.py:19
  35.2 5.0 %collective-permute-start.14 = (bf16[128,512]{1,0:T(8,128)(2,1)S(1)}, bf16[128,512]{1,0:T(8,128)(2,1)S(1)}, u32[]{:S(2)}, u32[]{:S(2)}) collective-permute-start(bf16[128,512]{1,0:T(8,128)(2,1)S(1)} %pad_maximum_fusion.3), channel_id=1, source_target_pairs={{0,2},{2,0},{4,6},{6,4},{8,10},{10,8},{12,14},{14,12},{1,3},{3,1},... | collective-permute-start | bytes 393224 | tf_op jit(solution)/shard_map/ppermute | solution.py:19
  36.1 5.0 %collective-permute-start.9 = (bf16[128,512]{1,0:T(8,128)(2,1)S(1)}, bf16[128,512]{1,0:T(8,128)(2,1)S(1)}, u32[]{:S(2)}, u32[]{:S(2)}) collective-permute-start(bf16[128,512]{1,0:T(8,128)(2,1)S(1)} %pad_maximum_fusion.2), channel_id=1, source_target_pairs={{0,4},{2,6},{4,0},{6,2},{8,12},{10,14},{12,8},{14,10},{1,5},{3,7},... | collective-permute-start | bytes 393224 | tf_op jit(solution)/shard_map/ppermute | solution.py:19
  37.3 5.0 %collective-permute-start.4 = (bf16[128,512]{1,0:T(8,128)(2,1)S(1)}, bf16[128,512]{1,0:T(8,128)(2,1)S(1)}, u32[]{:S(2)}, u32[]{:S(2)}) collective-permute-start(bf16[128,512]{1,0:T(8,128)(2,1)S(1)} %pad_maximum_fusion.1), channel_id=1, source_target_pairs={{0,2},{2,0},{4,6},{6,4},{8,10},{10,8},{12,14},{14,12},{1,3},{3,1},... | collective-permute-start | bytes 393224 | tf_op jit(solution)/shard_map/ppermute | solution.py:19
  42.9 1.6 %collective-permute-start.20 = (f32[512,128]{1,0:T(8,128)S(1)}, f32[512,128]{1,0:T(8,128)S(1)}, u32[]{:S(2)}, u32[]{:S(2)}) collective-permute-start(f32[512,128]{1,0:T(8,128)S(1)} %fusion.2.mine_ref), channel_id=1, source_target_pairs={{0,1},{1,0},{2,3},{3,2},{4,5},{5,4},{6,7},{7,6},{8,9},{9,8},{10,11... | collective-permute-start | bytes 786440 | tf_op jit(solution)/shard_map/ppermute | solution.py:19
  45.0 6.8 %collective-permute-start.24 = (f32[72,128]{1,0:T(8,128)S(1)}, f32[72,128]{1,0:T(8,128)S(1)}, u32[]{:S(2)}, u32[]{:S(2)}) collective-permute-start(f32[72,128]{1,0:T(8,128)S(1)} %get-tuple-element.17), channel_id=1, source_target_pairs={{0,10},{1,15},{2,8},{3,13},{4,14},{5,11},{6,12},{7,9},{8,2},{9,7},... | collective-permute-start | bytes 110600 | tf_op jit(solution)/shard_map/ppermute | solution.py:37
  48.4 5.5 %collective-permute-start.23 = (f32[72,128]{1,0:T(8,128)S(1)}, f32[72,128]{1,0:T(8,128)S(1)}, u32[]{:S(2)}, u32[]{:S(2)}) collective-permute-start(f32[72,128]{1,0:T(8,128)S(1)} %get-tuple-element.17), channel_id=1, source_target_pairs={{0,8},{1,13},{2,10},{3,15},{4,12},{5,9},{6,14},{7,11},{8,0},{9,5},... | collective-permute-start | bytes 110600 | tf_op jit(solution)/shard_map/ppermute | solution.py:37
  48.4 5.5 %collective-permute-start.22 = (f32[72,128]{1,0:T(8,128)S(1)}, f32[72,128]{1,0:T(8,128)S(1)}, u32[]{:S(2)}, u32[]{:S(2)}) collective-permute-start(f32[72,128]{1,0:T(8,128)S(1)} %get-tuple-element.17), channel_id=1, source_target_pairs={{0,2},{1,7},{2,0},{3,5},{4,6},{5,3},{6,4},{7,1},{8,10},{9,15},{10,... | collective-permute-start | bytes 110600 | tf_op jit(solution)/shard_map/ppermute | solution.py:37
  49.4 4.4 %collective-permute-start.21 = (f32[72,128]{1,0:T(8,128)S(1)}, f32[72,128]{1,0:T(8,128)S(1)}, u32[]{:S(2)}, u32[]{:S(2)}) collective-permute-start(f32[72,128]{1,0:T(8,128)S(1)} %get-tuple-element.17), channel_id=1, source_target_pairs={{1,5},{3,7},{5,1},{7,3},{9,13},{11,15},{13,9},{15,11},{17,21},{19,... | collective-permute-start | bytes 110600 | tf_op jit(solution)/shard_map/ppermute | solution.py:37
  53.9 1.3 %collective-permute-start.25 = (f32[72,128]{1,0:T(8,128)S(1)}, f32[72,128]{1,0:T(8,128)S(1)}, u32[]{:S(2)}, u32[]{:S(2)}) collective-permute-start(f32[72,128]{1,0:T(8,128)S(1)} %add_add_fusion), channel_id=1, source_target_pairs={{0,1},{1,0},{2,3},{3,2},{4,5},{5,4},{6,7},{7,6},{8,9},{9,8},{10,11... | collective-permute-start | bytes 110600 | tf_op jit(solution)/shard_map/ppermute | solution.py:19
  59.3 6.2 %collective-permute-start.26 = (bf16[2,2,16,1024]{3,2,0,1:T(8,128)(2,1)S(1)}, bf16[2,2,16,1024]{3,2,0,1:T(8,128)(2,1)S(1)}, u32[]{:S(2)}, u32[]{:S(2)}) collective-permute-start(bf16[2,2,16,1024]{3,2,0,1:T(8,128)(2,1)S(1)} %fusion.22), channel_id=1, source_target_pairs={{0,2},{2,0},{4,6},{6,4},{8,10},{10,8},{12,14},{14,12},{1,3},{3,1},... | collective-permute-start | bytes 393224 | tf_op jit(solution)/shard_map/ppermute | solution.py:19
  60.1 7.3 %collective-permute-start.29 = (bf16[2,2,16,1024]{3,2,0,1:T(8,128)(2,1)S(1)}, bf16[2,2,16,1024]{3,2,0,1:T(8,128)(2,1)S(1)}, u32[]{:S(2)}, u32[]{:S(2)}) collective-permute-start(bf16[2,2,16,1024]{3,2,0,1:T(8,128)(2,1)S(1)} %fusion.23), channel_id=1, source_target_pairs={{0,4},{2,6},{4,0},{6,2},{8,12},{10,14},{12,8},{14,10},{1,5},{3,7},... | collective-permute-start | bytes 393224 | tf_op jit(solution)/shard_map/ppermute | solution.py:19
  62.0 6.4 %collective-permute-start.32 = (bf16[2,2,16,1024]{3,2,0,1:T(8,128)(2,1)S(1)}, bf16[2,2,16,1024]{3,2,0,1:T(8,128)(2,1)S(1)}, u32[]{:S(2)}, u32[]{:S(2)}) collective-permute-start(bf16[2,2,16,1024]{3,2,0,1:T(8,128)(2,1)S(1)} %fusion.24), channel_id=1, source_target_pairs={{0,2},{2,0},{4,6},{6,4},{8,10},{10,8},{12,14},{14,12},{1,3},{3,1},... | collective-permute-start | bytes 393224 | tf_op jit(solution)/shard_map/ppermute | solution.py:19
  63.4 6.5 %collective-permute-start.35 = (bf16[2,2,16,1024]{3,2,0,1:T(8,128)(2,1)S(1)}, bf16[2,2,16,1024]{3,2,0,1:T(8,128)(2,1)S(1)}, u32[]{:S(2)}, u32[]{:S(2)}) collective-permute-start(bf16[2,2,16,1024]{3,2,0,1:T(8,128)(2,1)S(1)} %fusion.25), channel_id=1, source_target_pairs={{0,4},{2,6},{4,0},{6,2},{8,12},{10,14},{12,8},{14,10},{1,5},{3,7},... | collective-permute-start | bytes 393224 | tf_op jit(solution)/shard_map/ppermute | solution.py:19
  65.6 6.8 %collective-permute-start.27 = (f32[2,16,1024]{2,1,0:T(8,128)S(1)}, f32[2,16,1024]{2,1,0:T(8,128)S(1)}, u32[]{:S(2)}, u32[]{:S(2)}) collective-permute-start(f32[2,16,1024]{2,1,0:T(8,128)S(1)} %select_bitcast_fusion.3), channel_id=1, source_target_pairs={{0,4},{2,6},{4,0},{6,2},{8,12},{10,14},{12,8},{14,10},{1,5},{3,7},... | collective-permute-start | bytes 393224 | tf_op jit(solution)/shard_map/ppermute | solution.py:19
  67.5 8.3 %collective-permute-start.30 = (f32[2,16,1024]{2,1,0:T(8,128)S(1)}, f32[2,16,1024]{2,1,0:T(8,128)S(1)}, u32[]{:S(2)}, u32[]{:S(2)}) collective-permute-start(f32[2,16,1024]{2,1,0:T(8,128)S(1)} %select_bitcast_fusion.2), channel_id=1, source_target_pairs={{0,2},{2,0},{4,6},{6,4},{8,10},{10,8},{12,14},{14,12},{1,3},{3,1},... | collective-permute-start | bytes 393224 | tf_op jit(solution)/shard_map/ppermute | solution.py:19
  68.4 7.9 %collective-permute-start.33 = (f32[2,16,1024]{2,1,0:T(8,128)S(1)}, f32[2,16,1024]{2,1,0:T(8,128)S(1)}, u32[]{:S(2)}, u32[]{:S(2)}) collective-permute-start(f32[2,16,1024]{2,1,0:T(8,128)S(1)} %select_bitcast_fusion.1), channel_id=1, source_target_pairs={{0,4},{2,6},{4,0},{6,2},{8,12},{10,14},{12,8},{14,10},{1,5},{3,7},... | collective-permute-start | bytes 393224 | tf_op jit(solution)/shard_map/ppermute | solution.py:19
  69.9 9.0 %collective-permute-start.36 = (f32[2,16,1024]{2,1,0:T(8,128)S(1)}, f32[2,16,1024]{2,1,0:T(8,128)S(1)}, u32[]{:S(2)}, u32[]{:S(2)}) collective-permute-start(f32[2,16,1024]{2,1,0:T(8,128)S(1)} %select_bitcast_fusion), channel_id=1, source_target_pairs={{0,2},{2,0},{4,6},{6,4},{8,10},{10,8},{12,14},{14,12},{1,3},{3,1},... | collective-permute-start | bytes 393224 | tf_op jit(solution)/shard_map/ppermute | solution.py:19
  72.4 7.1 %collective-permute-start.28 = (bf16[16,1024]{1,0:T(8,128)(2,1)S(1)}, bf16[16,1024]{1,0:T(8,128)(2,1)S(1)}, u32[]{:S(2)}, u32[]{:S(2)}) collective-permute-start(bf16[16,1024]{1,0:T(8,128)(2,1)S(1)} %fusion.30), channel_id=1, source_target_pairs={{0,8},{2,10},{4,12},{6,14},{8,0},{10,2},{12,4},{14,6},{1,9},{3,11}... | collective-permute-start | bytes 98312 | tf_op jit(solution)/shard_map/ppermute | solution.py:19
  75.8 5.3 %collective-permute-start.31 = (bf16[16,1024]{1,0:T(8,128)(2,1)S(1)}, bf16[16,1024]{1,0:T(8,128)(2,1)S(1)}, u32[]{:S(2)}, u32[]{:S(2)}) collective-permute-start(bf16[16,1024]{1,0:T(8,128)(2,1)S(1)} %fusion.31), channel_id=1, source_target_pairs={{0,8},{2,10},{4,12},{6,14},{8,0},{10,2},{12,4},{14,6},{1,9},{3,11}... | collective-permute-start | bytes 98312 | tf_op jit(solution)/shard_map/ppermute | solution.py:19
  76.4 5.5 %collective-permute-start.34 = (bf16[16,1024]{1,0:T(8,128)(2,1)S(1)}, bf16[16,1024]{1,0:T(8,128)(2,1)S(1)}, u32[]{:S(2)}, u32[]{:S(2)}) collective-permute-start(bf16[16,1024]{1,0:T(8,128)(2,1)S(1)} %fusion.32), channel_id=1, source_target_pairs={{0,8},{2,10},{4,12},{6,14},{8,0},{10,2},{12,4},{14,6},{1,9},{3,11}... | collective-permute-start | bytes 98312 | tf_op jit(solution)/shard_map/ppermute | solution.py:19
  79.0 5.1 %collective-permute-start.37 = (bf16[16,1024]{1,0:T(8,128)(2,1)S(1)}, bf16[16,1024]{1,0:T(8,128)(2,1)S(1)}, u32[]{:S(2)}, u32[]{:S(2)}) collective-permute-start(bf16[16,1024]{1,0:T(8,128)(2,1)S(1)} %fusion.33), channel_id=1, source_target_pairs={{0,8},{2,10},{4,12},{6,14},{8,0},{10,2},{12,4},{14,6},{1,9},{3,11}... | collective-permute-start | bytes 98312 | tf_op jit(solution)/shard_map/ppermute | solution.py:19

commit v29 on v28

--- a/solution.py
+++ b/solution.py
@@ -47,13 +47,13 @@
     rows, cols = value.shape[0] >> len(order), value.shape[1]
     total = value.reshape([2] * len(order) + [rows, cols])
     left = sorted(order, reverse=True)
-    for step, bit in enumerate(order):
+    for bit in order:
         dim = left.index(bit)
         left.remove(bit)
         low = lax.index_in_dim(total, 0, dim, keepdims=False)
         high = lax.index_in_dim(total, 1, dim, keepdims=False)
         upper = bit_of(axis, bit) == 1
-        send = jnp.where(upper, low, high).astype(LINK_TYPES[min(step, 2)])
+        send = jnp.where(upper, low, high).astype(jnp.bfloat16)
         landed = swap(send, axis, 1 << bit)
         total = jnp.where(upper, high, low) + landed.astype(jnp.float32)
     return total

time: 85 us -> 83.3 us (0.980)
  waiting for transfers between devices: 23.3 us -> 21.4 us
    ppermute x34, waiting for transfers between devices: 19.6 us -> 17.7 us  [swap(): return lax.ppermute(value, axis, [(i, i ^ distance) for i in range(size)])]
  transfers between devices with their start and end apart: 38 -> 38, of which waited for: 21 -> 20; matrix products, arithmetic and copies ran while one was open for 3% -> 3% of each run, Pallas kernels for 2% -> 2%
where the time goes in v29:
time: 83.3 us; the launch traced here: 83.1 us
  starting transfers between devices  47 us (56%)
  waiting for transfers between devices  21.4 us (26%)
  Pallas kernels  8.67 us (10%)
  other arithmetic  2.09 us (3%)
  matrix products  1.77 us (2%)
  between operations  1.1 us (1%)
  local copies, waits for them, and re-layouts  1.05 us (1%)
    ppermute x34, starting transfers between devices, swap(): return lax.ppermute(value, axis, [(i, i ^ distance) for i in range(size)])  41.9 us
    ppermute x34, waiting for transfers between devices, swap(): return lax.ppermute(value, axis, [(i, i ^ distance) for i in range(size)])  17.7 us
    ppermute x4, starting transfers between devices, row_sum(): terms.append(lax.ppermute(value, ('row', 'col'), pairs))  5.1 us
    pallas_call x1, Pallas kernels, make_basis(): pl.pallas_call(functools.partial(basis_kernel, root_rows), out_shape=[jax...  4.1 us
    pallas_call x2, Pallas kernels, first_product(): pl.pallas_call(functools.partial(sketch_kernel, begin), out_shape=[jax.Sh...  4.07 us
    ppermute x4, waiting for transfers between devices, row_sum(): terms.append(lax.ppermute(value, ('row', 'col'), pairs))  3.74 us
    dot_general x4, matrix products, per_device(): lax.dot_general(activations[:, span], shared, (((1,), (1,)), ((), ())), p...  1.77 us
  transfers between devices with their start and end apart: 38, of which 20 were waited for; matrix products, arithmetic and copies ran while one was open for 3% of the time, Pallas kernels for 2%

profile of v29, /device:TPU:0, one launch (start us, length us, event | category | flops | bytes accessed | tf_op | source)
XLA Modules:
  0.0 83.1 jit_solution(97917383484356326)
XLA Ops:
  0.7 0.9 %copy-done = bf16[512,128]{1,0:T(8,128)(2,1)S(1)} copy-done((bf16[512,128]{1,0:T(8,128)(2,1)S(1)}, bf16[512,128]{1,0:T(8,128)(2,1)}, u32[]{:S(2)}) %copy-start) | copy-done | bytes 131096
  1.6 2.1 %first_product.3 = (f32[128,1024]{1,0:T(8,128)S(1)}, f32[128,1024]{1,0:T(8,128)S(1)}) custom-call(bf16[512,128]{1,0:T(8,128)(2,1)S(1)} %copy-done, bf16[512,4096]{1,0:T(8,128)(2,1)} %slab_ref.5), custom_call_target="tpu_custom_call" | custom-call | flops 268435456 | bytes 2097152 | tf_op jit(solution)/shard_map/first_product/pallas_call | solution.py:118
  3.6 3.1 %collective-permute-start.15 = (bf16[128,512]{1,0:T(8,128)(2,1)S(1)}, bf16[128,512]{1,0:T(8,128)(2,1)S(1)}, u32[]{:S(2)}, u32[]{:S(2)}) collective-permute-start(bf16[128,512]{1,0:T(8,128)(2,1)S(1)} %select_convert_fusion.4), channel_id=1, source_target_pairs={{0,4},{2,6},{4,0},{6,2},{8,12},{10,14},{12,8},{14,10},{1,5},{3,7},... | collective-permute-start | bytes 393224 | tf_op jit(solution)/shard_map/ppermute | solution.py:19
  6.8 1.6 %collective-permute-start.10 = (bf16[128,512]{1,0:T(8,128)(2,1)S(1)}, bf16[128,512]{1,0:T(8,128)(2,1)S(1)}, u32[]{:S(2)}, u32[]{:S(2)}) collective-permute-start(bf16[128,512]{1,0:T(8,128)(2,1)S(1)} %select_convert_fusion.5), channel_id=1, source_target_pairs={{0,2},{2,0},{4,6},{6,4},{8,10},{10,8},{12,14},{14,12},{1,3},{3,1},... | collective-permute-start | bytes 393224 | tf_op jit(solution)/shard_map/ppermute | solution.py:19
  8.3 2.0 %first_product.2 = (f32[128,1024]{1,0:T(8,128)S(1)}, f32[128,1024]{1,0:T(8,128)S(1)}) custom-call(bf16[512,128]{1,0:T(8,128)(2,1)S(1)} %copy-done.1, bf16[512,4096]{1,0:T(8,128)(2,1)} %slab_ref.5), custom_call_target="tpu_custom_call" | custom-call | flops 268435456 | bytes 2097152 | tf_op jit(solution)/shard_map/first_product/pallas_call | solution.py:118
  11.2 2.0 %collective-permute-start.16 = (f32[128,256]{1,0:T(8,128)S(1)}, f32[128,256]{1,0:T(8,128)S(1)}, u32[]{:S(2)}, u32[]{:S(2)}) collective-permute-start(f32[128,256]{1,0:T(8,128)S(1)} %slice_select_fusion), channel_id=1, source_target_pairs={{0,2},{2,0},{4,6},{6,4},{8,10},{10,8},{12,14},{14,12},{1,3},{3,1},... | collective-permute-start | bytes 393224 | tf_op jit(solution)/shard_map/ppermute | solution.py:19
  13.3 1.6 %collective-permute-start.11 = (f32[128,256]{1,0:T(8,128)S(1)}, f32[128,256]{1,0:T(8,128)S(1)}, u32[]{:S(2)}, u32[]{:S(2)}) collective-permute-start(f32[128,256]{1,0:T(8,128)S(1)} %slice_select_fusion.1), channel_id=1, source_target_pairs={{0,4},{2,6},{4,0},{6,2},{8,12},{10,14},{12,8},{14,10},{1,5},{3,7},... | collective-permute-start | bytes 393224 | tf_op jit(solution)/shard_map/ppermute | solution.py:19
  14.9 1.6 %collective-permute-done.5 = bf16[128,512]{1,0:T(8,128)(2,1)S(1)} collective-permute-done((bf16[128,512]{1,0:T(8,128)(2,1)S(1)}, bf16[128,512]{1,0:T(8,128)(2,1)S(1)}, u32[]{:S(2)}, u32[]{:S(2)}) %collective-permute-start.5) | collective-permute-done | bytes 131104 | tf_op jit(solution)/shard_map/ppermute | solution.py:19
  16.6 0.8 collective-permute-start.6
  17.4 1.8 %collective-permute-start.1 = (f32[128,256]{1,0:T(8,128)S(1)}, f32[128,256]{1,0:T(8,128)S(1)}, u32[]{:S(2)}, u32[]{:S(2)}) collective-permute-start(f32[128,256]{1,0:T(8,128)S(1)} %slice_select_fusion.3), channel_id=1, source_target_pairs={{0,4},{2,6},{4,0},{6,2},{8,12},{10,14},{12,8},{14,10},{1,5},{3,7},... | collective-permute-start | bytes 393224 | tf_op jit(solution)/shard_map/ppermute | solution.py:19
  19.6 2.7 %collective-permute-start.17 = (bf16[128,256]{1,0:T(8,128)(2,1)S(1)}, bf16[128,256]{1,0:T(8,128)(2,1)S(1)}, u32[]{:S(2)}, u32[]{:S(2)}) collective-permute-start(bf16[128,256]{1,0:T(8,128)(2,1)S(1)} %get-tuple-element.30), channel_id=1, source_target_pairs={{0,8},{2,10},{4,12},{6,14},{8,0},{10,2},{12,4},{14,6},{1,9},{3,11}... | collective-permute-start | bytes 196616 | tf_op jit(solution)/shard_map/ppermute | solution.py:19
  22.8 2.7 %collective-permute-start.7 = (bf16[128,256]{1,0:T(8,128)(2,1)S(1)}, bf16[128,256]{1,0:T(8,128)(2,1)S(1)}, u32[]{:S(2)}, u32[]{:S(2)}) collective-permute-start(bf16[128,256]{1,0:T(8,128)(2,1)S(1)} %get-tuple-element.26), channel_id=1, source_target_pairs={{0,8},{2,10},{4,12},{6,14},{8,0},{10,2},{12,4},{14,6},{1,9},{3,11}... | collective-permute-start | bytes 196616 | tf_op jit(solution)/shard_map/ppermute | solution.py:19
  25.4 0.7 collective-permute-start.2
  26.1 1.3 %collective-permute-done.17 = bf16[128,256]{1,0:T(8,128)(2,1)S(1)} collective-permute-done((bf16[128,256]{1,0:T(8,128)(2,1)S(1)}, bf16[128,256]{1,0:T(8,128)(2,1)S(1)}, u32[]{:S(2)}, u32[]{:S(2)}) %collective-permute-start.17) | collective-permute-done | bytes 65568 | tf_op jit(solution)/shard_map/ppermute | solution.py:19
  27.5 0.9 %collective-permute-start.18 = (bf16[128,256]{1,0:T(8,128)(2,1)S(1)}, bf16[128,256]{1,0:T(8,128)(2,1)S(1)}, u32[]{:S(2)}, u32[]{:S(2)}) collective-permute-start(bf16[128,256]{1,0:T(8,128)(2,1)S(1)} %multiply_convert_fusion), channel_id=1, source_target_pairs={{0,2},{2,0},{4,6},{6,4},{8,10},{10,8},{12,14},{14,12},{1,3},{3,1},... | collective-permute-start | bytes 196616 | tf_op jit(solution)/shard_map/ppermute | solution.py:19
  28.4 1.7 %collective-permute-done.12 = bf16[128,256]{1,0:T(8,128)(2,1)S(1)} collective-permute-done((bf16[128,256]{1,0:T(8,128)(2,1)S(1)}, bf16[128,256]{1,0:T(8,128)(2,1)S(1)}, u32[]{:S(2)}, u32[]{:S(2)}) %collective-permute-start.12) | collective-permute-done | bytes 65568 | tf_op jit(solution)/shard_map/ppermute | solution.py:19
  30.8 0.9 %collective-permute-start.8 = (bf16[128,256]{1,0:T(8,128)(2,1)S(1)}, bf16[128,256]{1,0:T(8,128)(2,1)S(1)}, u32[]{:S(2)}, u32[]{:S(2)}) collective-permute-start(bf16[128,256]{1,0:T(8,128)(2,1)S(1)} %multiply_convert_fusion.2), channel_id=1, source_target_pairs={{0,2},{2,0},{4,6},{6,4},{8,10},{10,8},{12,14},{14,12},{1,3},{3,1},... | collective-permute-start | bytes 196616 | tf_op jit(solution)/shard_map/ppermute | solution.py:19
  32.2 1.0 %collective-permute-start.3 = (bf16[128,256]{1,0:T(8,128)(2,1)S(1)}, bf16[128,256]{1,0:T(8,128)(2,1)S(1)}, u32[]{:S(2)}, u32[]{:S(2)}) collective-permute-start(bf16[128,256]{1,0:T(8,128)(2,1)S(1)} %multiply_convert_fusion.3), channel_id=1, source_target_pairs={{0,4},{2,6},{4,0},{6,2},{8,12},{10,14},{12,8},{14,10},{1,5},{3,7},... | collective-permute-start | bytes 196616 | tf_op jit(solution)/shard_map/ppermute | solution.py:19
  33.2 1.2 %collective-permute-start.19 = (bf16[128,512]{1,0:T(8,128)(2,1)S(1)}, bf16[128,512]{1,0:T(8,128)(2,1)S(1)}, u32[]{:S(2)}, u32[]{:S(2)}) collective-permute-start(bf16[128,512]{1,0:T(8,128)(2,1)S(1)} %pad_maximum_fusion.4), channel_id=1, source_target_pairs={{0,4},{2,6},{4,0},{6,2},{8,12},{10,14},{12,8},{14,10},{1,5},{3,7},... | collective-permute-start | bytes 393224 | tf_op jit(solution)/shard_map/ppermute | solution.py:19
  34.4 0.7 collective-permute-done.13
  35.2 0.9 %collective-permute-start.14 = (bf16[128,512]{1,0:T(8,128)(2,1)S(1)}, bf16[128,512]{1,0:T(8,128)(2,1)S(1)}, u32[]{:S(2)}, u32[]{:S(2)}) collective-permute-start(bf16[128,512]{1,0:T(8,128)(2,1)S(1)} %pad_maximum_fusion.3), channel_id=1, source_target_pairs={{0,2},{2,0},{4,6},{6,4},{8,10},{10,8},{12,14},{14,12},{1,3},{3,1},... | collective-permute-start | bytes 393224 | tf_op jit(solution)/shard_map/ppermute | solution.py:19
  36.1 1.1 %collective-permute-start.9 = (bf16[128,512]{1,0:T(8,128)(2,1)S(1)}, bf16[128,512]{1,0:T(8,128)(2,1)S(1)}, u32[]{:S(2)}, u32[]{:S(2)}) collective-permute-start(bf16[128,512]{1,0:T(8,128)(2,1)S(1)} %pad_maximum_fusion.2), channel_id=1, source_target_pairs={{0,4},{2,6},{4,0},{6,2},{8,12},{10,14},{12,8},{14,10},{1,5},{3,7},... | collective-permute-start | bytes 393224 | tf_op jit(solution)/shard_map/ppermute | solution.py:19
  37.3 0.9 %collective-permute-start.4 = (bf16[128,512]{1,0:T(8,128)(2,1)S(1)}, bf16[128,512]{1,0:T(8,128)(2,1)S(1)}, u32[]{:S(2)}, u32[]{:S(2)}) collective-permute-start(bf16[128,512]{1,0:T(8,128)(2,1)S(1)} %pad_maximum_fusion.1), channel_id=1, source_target_pairs={{0,2},{2,0},{4,6},{6,4},{8,10},{10,8},{12,14},{14,12},{1,3},{3,1},... | collective-permute-start | bytes 393224 | tf_op jit(solution)/shard_map/ppermute | solution.py:19
  38.2 0.8 collective-permute-done.19
  41.6 0.8 collective-permute-done.4
  43.0 1.5 %collective-permute-done.20.other_ref = f32[512,128]{1,0:T(8,128)S(1)} collective-permute-done((f32[512,128]{1,0:T(8,128)S(1)}, f32[512,128]{1,0:T(8,128)S(1)}, u32[]{:S(2)}, u32[]{:S(2)}) %collective-permute-start.20) | collective-permute-done | bytes 262176 | tf_op jit(solution)/shard_map/ppermute | solution.py:19
  45.0 3.4 %collective-permute-start.24 = (f32[72,128]{1,0:T(8,128)S(1)}, f32[72,128]{1,0:T(8,128)S(1)}, u32[]{:S(2)}, u32[]{:S(2)}) collective-permute-start(f32[72,128]{1,0:T(8,128)S(1)} %get-tuple-element.17), channel_id=1, source_target_pairs={{0,10},{1,15},{2,8},{3,13},{4,14},{5,11},{6,12},{7,9},{8,2},{9,7},... | collective-permute-start | bytes 110600 | tf_op jit(solution)/shard_map/ppermute | solution.py:37
  48.4 1.1 %collective-permute-start.22 = (f32[72,128]{1,0:T(8,128)S(1)}, f32[72,128]{1,0:T(8,128)S(1)}, u32[]{:S(2)}, u32[]{:S(2)}) collective-permute-start(f32[72,128]{1,0:T(8,128)S(1)} %get-tuple-element.17), channel_id=1, source_target_pairs={{0,2},{1,7},{2,0},{3,5},{4,6},{5,3},{6,4},{7,1},{8,10},{9,15},{10,... | collective-permute-start | bytes 110600 | tf_op jit(solution)/shard_map/ppermute | solution.py:37
  50.1 1.7 %collective-permute-done.24 = f32[72,128]{1,0:T(8,128)S(1)} collective-permute-done((f32[72,128]{1,0:T(8,128)S(1)}, f32[72,128]{1,0:T(8,128)S(1)}, u32[]{:S(2)}, u32[]{:S(2)}) %collective-permute-start.24) | collective-permute-done | bytes 36896 | tf_op jit(solution)/shard_map/ppermute | solution.py:37
  51.8 2.0 %collective-permute-done.23 = f32[72,128]{1,0:T(8,128)S(1)} collective-permute-done((f32[72,128]{1,0:T(8,128)S(1)}, f32[72,128]{1,0:T(8,128)S(1)}, u32[]{:S(2)}, u32[]{:S(2)}) %collective-permute-start.23) | collective-permute-done | bytes 36896 | tf_op jit(solution)/shard_map/ppermute | solution.py:37
  54.1 1.0 %collective-permute-done.25 = f32[72,128]{1,0:T(8,128)S(1)} collective-permute-done((f32[72,128]{1,0:T(8,128)S(1)}, f32[72,128]{1,0:T(8,128)S(1)}, u32[]{:S(2)}, u32[]{:S(2)}) %collective-permute-start.25) | collective-permute-done | bytes 36896 | tf_op jit(solution)/shard_map/ppermute | solution.py:19
  55.2 4.1 %make_basis.1 = (f32[512,128]{1,0:T(8,128)}, f32[128,1024]{1,0:T(8,128)S(1)}, f32[128,1024]{1,0:T(8,128)S(1)}, f32[128,1024]{1,0:T(8,128)S(1)}, f32[128,1024]{1,0:T(8,128)S(1)}) custom-call(f32[72,128]{1,0:T(8,128)S(1)} %add.116.gram_ref, f32[128,512]{1,0:T(8,128)S(1)} %get-tuple-element.18.sketch_ref, bf16[512,4096]{1,0:T(8,128)(2,1)} %slab_ref.5), custom_call_target="tpu_custom_call" | custom-call | tf_op jit(solution)/shard_map/make_basis/pallas_call | solution.py:280
  59.3 0.7 collective-permute-start.26
  60.1 1.8 %collective-permute-start.29 = (bf16[2,2,16,1024]{3,2,0,1:T(8,128)(2,1)S(1)}, bf16[2,2,16,1024]{3,2,0,1:T(8,128)(2,1)S(1)}, u32[]{:S(2)}, u32[]{:S(2)}) collective-permute-start(bf16[2,2,16,1024]{3,2,0,1:T(8,128)(2,1)S(1)} %fusion.23), channel_id=1, source_target_pairs={{0,4},{2,6},{4,0},{6,2},{8,12},{10,14},{12,8},{14,10},{1,5},{3,7},... | collective-permute-start | bytes 393224 | tf_op jit(solution)/shard_map/ppermute | solution.py:19
  62.0 1.3 %collective-permute-start.32 = (bf16[2,2,16,1024]{3,2,0,1:T(8,128)(2,1)S(1)}, bf16[2,2,16,1024]{3,2,0,1:T(8,128)(2,1)S(1)}, u32[]{:S(2)}, u32[]{:S(2)}) collective-permute-start(bf16[2,2,16,1024]{3,2,0,1:T(8,128)(2,1)S(1)} %fusion.24), channel_id=1, source_target_pairs={{0,2},{2,0},{4,6},{6,4},{8,10},{10,8},{12,14},{14,12},{1,3},{3,1},... | collective-permute-start | bytes 393224 | tf_op jit(solution)/shard_map/ppermute | solution.py:19
  63.9 1.6 %collective-permute-done.26 = bf16[2,2,16,1024]{3,2,0,1:T(8,128)(2,1)S(1)} collective-permute-done((bf16[2,2,16,1024]{3,2,0,1:T(8,128)(2,1)S(1)}, bf16[2,2,16,1024]{3,2,0,1:T(8,128)(2,1)S(1)}, u32[]{:S(2)}, u32[]{:S(2)}) %collective-permute-start.26) | collective-permute-done | bytes 131104 | tf_op jit(solution)/shard_map/ppermute | solution.py:19
  65.6 1.9 %collective-permute-start.27 = (bf16[2,16,1024]{2,1,0:T(8,128)(2,1)S(1)}, bf16[2,16,1024]{2,1,0:T(8,128)(2,1)S(1)}, u32[]{:S(2)}, u32[]{:S(2)}) collective-permute-start(bf16[2,16,1024]{2,1,0:T(8,128)(2,1)S(1)} %fusion.26), channel_id=1, source_target_pairs={{0,4},{2,6},{4,0},{6,2},{8,12},{10,14},{12,8},{14,10},{1,5},{3,7},... | collective-permute-start | bytes 196616 | tf_op jit(solution)/shard_map/ppermute | solution.py:19
  67.5 0.8 %collective-permute-start.30 = (bf16[2,16,1024]{2,1,0:T(8,128)(2,1)S(1)}, bf16[2,16,1024]{2,1,0:T(8,128)(2,1)S(1)}, u32[]{:S(2)}, u32[]{:S(2)}) collective-permute-start(bf16[2,16,1024]{2,1,0:T(8,128)(2,1)S(1)} %fusion.27), channel_id=1, source_target_pairs={{0,2},{2,0},{4,6},{6,4},{8,10},{10,8},{12,14},{14,12},{1,3},{3,1},... | collective-permute-start | bytes 196616 | tf_op jit(solution)/shard_map/ppermute | solution.py:19
  68.4 1.4 %collective-permute-start.33 = (bf16[2,16,1024]{2,1,0:T(8,128)(2,1)S(1)}, bf16[2,16,1024]{2,1,0:T(8,128)(2,1)S(1)}, u32[]{:S(2)}, u32[]{:S(2)}) collective-permute-start(bf16[2,16,1024]{2,1,0:T(8,128)(2,1)S(1)} %fusion.28), channel_id=1, source_target_pairs={{0,4},{2,6},{4,0},{6,2},{8,12},{10,14},{12,8},{14,10},{1,5},{3,7},... | collective-permute-start | bytes 196616 | tf_op jit(solution)/shard_map/ppermute | solution.py:19
  69.9 0.8 collective-permute-start.36
  70.8 3.4 %collective-permute-start.28 = (bf16[16,1024]{1,0:T(8,128)(2,1)S(1)}, bf16[16,1024]{1,0:T(8,128)(2,1)S(1)}, u32[]{:S(2)}, u32[]{:S(2)}) collective-permute-start(bf16[16,1024]{1,0:T(8,128)(2,1)S(1)} %fusion.34), channel_id=1, source_target_pairs={{0,8},{2,10},{4,12},{6,14},{8,0},{10,2},{12,4},{14,6},{1,9},{3,11}... | collective-permute-start | bytes 98312 | tf_op jit(solution)/shard_map/ppermute | solution.py:19
  74.2 0.8 collective-permute-start.31
  75.0 2.3 %collective-permute-start.34 = (bf16[16,1024]{1,0:T(8,128)(2,1)S(1)}, bf16[16,1024]{1,0:T(8,128)(2,1)S(1)}, u32[]{:S(2)}, u32[]{:S(2)}) collective-permute-start(bf16[16,1024]{1,0:T(8,128)(2,1)S(1)} %fusion.36), channel_id=1, source_target_pairs={{0,8},{2,10},{4,12},{6,14},{8,0},{10,2},{12,4},{14,6},{1,9},{3,11}... | collective-permute-start | bytes 98312 | tf_op jit(solution)/shard_map/ppermute | solution.py:19
  77.4 0.8 collective-permute-start.37
  78.2 1.8 %collective-permute-done.31 = bf16[16,1024]{1,0:T(8,128)(2,1)S(1)} collective-permute-done((bf16[16,1024]{1,0:T(8,128)(2,1)S(1)}, bf16[16,1024]{1,0:T(8,128)(2,1)S(1)}, u32[]{:S(2)}, u32[]{:S(2)}) %collective-permute-start.31) | collective-permute-done | bytes 32800 | tf_op jit(solution)/shard_map/ppermute | solution.py:19
  79.9 0.7 collective-permute-done.34
  80.6 1.7 %collective-permute-done.37 = bf16[16,1024]{1,0:T(8,128)(2,1)S(1)} collective-permute-done((bf16[16,1024]{1,0:T(8,128)(2,1)S(1)}, bf16[16,1024]{1,0:T(8,128)(2,1)S(1)}, u32[]{:S(2)}, u32[]{:S(2)}) %collective-permute-start.37) | collective-permute-done | bytes 32800 | tf_op jit(solution)/shard_map/ppermute | solution.py:19
  82.4 0.7 pad_maximum_fusion
  (105 shorter events, 9.3 us)
Async XLA Ops:
  0.6 0.9 %copy-start = (bf16[512,128]{1,0:T(8,128)(2,1)S(1)}, bf16[512,128]{1,0:T(8,128)(2,1)}, u32[]{:S(2)}) copy-start(bf16[512,128]{1,0:T(8,128)(2,1)} %start_ref.3) | copy-start | bytes 393220
  1.6 6.8 %copy-start.1 = (bf16[512,128]{1,0:T(8,128)(2,1)S(1)}, bf16[512,128]{1,0:T(8,128)(2,1)}, u32[]{:S(2)}) copy-start(bf16[512,128]{1,0:T(8,128)(2,1)} %start_ref.3) | copy-start | bytes 393220
  3.6 7.5 %collective-permute-start.15 = (bf16[128,512]{1,0:T(8,128)(2,1)S(1)}, bf16[128,512]{1,0:T(8,128)(2,1)S(1)}, u32[]{:S(2)}, u32[]{:S(2)}) collective-permute-start(bf16[128,512]{1,0:T(8,128)(2,1)S(1)} %select_convert_fusion.4), channel_id=1, source_target_pairs={{0,4},{2,6},{4,0},{6,2},{8,12},{10,14},{12,8},{14,10},{1,5},{3,7},... | collective-permute-start | bytes 393224 | tf_op jit(solution)/shard_map/ppermute | solution.py:19
  6.8 6.4 %collective-permute-start.10 = (bf16[128,512]{1,0:T(8,128)(2,1)S(1)}, bf16[128,512]{1,0:T(8,128)(2,1)S(1)}, u32[]{:S(2)}, u32[]{:S(2)}) collective-permute-start(bf16[128,512]{1,0:T(8,128)(2,1)S(1)} %select_convert_fusion.5), channel_id=1, source_target_pairs={{0,2},{2,0},{4,6},{6,4},{8,10},{10,8},{12,14},{14,12},{1,3},{3,1},... | collective-permute-start | bytes 393224 | tf_op jit(solution)/shard_map/ppermute | solution.py:19
  10.4 6.1 %collective-permute-start.5 = (bf16[128,512]{1,0:T(8,128)(2,1)S(1)}, bf16[128,512]{1,0:T(8,128)(2,1)S(1)}, u32[]{:S(2)}, u32[]{:S(2)}) collective-permute-start(bf16[128,512]{1,0:T(8,128)(2,1)S(1)} %select_convert_fusion.6), channel_id=1, source_target_pairs={{0,4},{2,6},{4,0},{6,2},{8,12},{10,14},{12,8},{14,10},{1,5},{3,7},... | collective-permute-start | bytes 393224 | tf_op jit(solution)/shard_map/ppermute | solution.py:19
  10.9 6.4 %collective-permute-start = (bf16[128,512]{1,0:T(8,128)(2,1)S(1)}, bf16[128,512]{1,0:T(8,128)(2,1)S(1)}, u32[]{:S(2)}, u32[]{:S(2)}) collective-permute-start(bf16[128,512]{1,0:T(8,128)(2,1)S(1)} %select_convert_fusion.7), channel_id=1, source_target_pairs={{0,2},{2,0},{4,6},{6,4},{8,10},{10,8},{12,14},{14,12},{1,3},{3,1},... | collective-permute-start | bytes 393224 | tf_op jit(solution)/shard_map/ppermute | solution.py:19
  11.2 8.4 %collective-permute-start.16 = (f32[128,256]{1,0:T(8,128)S(1)}, f32[128,256]{1,0:T(8,128)S(1)}, u32[]{:S(2)}, u32[]{:S(2)}) collective-permute-start(f32[128,256]{1,0:T(8,128)S(1)} %slice_select_fusion), channel_id=1, source_target_pairs={{0,2},{2,0},{4,6},{6,4},{8,10},{10,8},{12,14},{14,12},{1,3},{3,1},... | collective-permute-start | bytes 393224 | tf_op jit(solution)/shard_map/ppermute | solution.py:19
  13.2 25.8 %copy-start.2 = (bf16[512,4096]{1,0:T(8,128)(2,1)S(1)}, bf16[512,4096]{1,0:T(8,128)(2,1)}, u32[]{:S(2)}) copy-start(bf16[512,4096]{1,0:T(8,128)(2,1)} %slab_ref.5) | copy-start | bytes 12582916
  13.3 9.0 %collective-permute-start.11 = (f32[128,256]{1,0:T(8,128)S(1)}, f32[128,256]{1,0:T(8,128)S(1)}, u32[]{:S(2)}, u32[]{:S(2)}) collective-permute-start(f32[128,256]{1,0:T(8,128)S(1)} %slice_select_fusion.1), channel_id=1, source_target_pairs={{0,4},{2,6},{4,0},{6,2},{8,12},{10,14},{12,8},{14,10},{1,5},{3,7},... | collective-permute-start | bytes 393224 | tf_op jit(solution)/shard_map/ppermute | solution.py:19
  16.6 6.2 %collective-permute-start.6 = (f32[128,256]{1,0:T(8,128)S(1)}, f32[128,256]{1,0:T(8,128)S(1)}, u32[]{:S(2)}, u32[]{:S(2)}) collective-permute-start(f32[128,256]{1,0:T(8,128)S(1)} %slice_select_fusion.2), channel_id=1, source_target_pairs={{0,2},{2,0},{4,6},{6,4},{8,10},{10,8},{12,14},{14,12},{1,3},{3,1},... | collective-permute-start | bytes 393224 | tf_op jit(solution)/shard_map/ppermute | solution.py:19
  17.4 8.0 %collective-permute-start.1 = (f32[128,256]{1,0:T(8,128)S(1)}, f32[128,256]{1,0:T(8,128)S(1)}, u32[]{:S(2)}, u32[]{:S(2)}) collective-permute-start(f32[128,256]{1,0:T(8,128)S(1)} %slice_select_fusion.3), channel_id=1, source_target_pairs={{0,4},{2,6},{4,0},{6,2},{8,12},{10,14},{12,8},{14,10},{1,5},{3,7},... | collective-permute-start | bytes 393224 | tf_op jit(solution)/shard_map/ppermute | solution.py:19
  19.6 7.8 %collective-permute-start.17 = (bf16[128,256]{1,0:T(8,128)(2,1)S(1)}, bf16[128,256]{1,0:T(8,128)(2,1)S(1)}, u32[]{:S(2)}, u32[]{:S(2)}) collective-permute-start(bf16[128,256]{1,0:T(8,128)(2,1)S(1)} %get-tuple-element.30), channel_id=1, source_target_pairs={{0,8},{2,10},{4,12},{6,14},{8,0},{10,2},{12,4},{14,6},{1,9},{3,11}... | collective-permute-start | bytes 196616 | tf_op jit(solution)/shard_map/ppermute | solution.py:19
  22.3 7.8 %collective-permute-start.12 = (bf16[128,256]{1,0:T(8,128)(2,1)S(1)}, bf16[128,256]{1,0:T(8,128)(2,1)S(1)}, u32[]{:S(2)}, u32[]{:S(2)}) collective-permute-start(bf16[128,256]{1,0:T(8,128)(2,1)S(1)} %get-tuple-element.28), channel_id=1, source_target_pairs={{0,8},{2,10},{4,12},{6,14},{8,0},{10,2},{12,4},{14,6},{1,9},{3,11}... | collective-permute-start | bytes 196616 | tf_op jit(solution)/shard_map/ppermute | solution.py:19
  22.8 8.0 %collective-permute-start.7 = (bf16[128,256]{1,0:T(8,128)(2,1)S(1)}, bf16[128,256]{1,0:T(8,128)(2,1)S(1)}, u32[]{:S(2)}, u32[]{:S(2)}) collective-permute-start(bf16[128,256]{1,0:T(8,128)(2,1)S(1)} %get-tuple-element.26), channel_id=1, source_target_pairs={{0,8},{2,10},{4,12},{6,14},{8,0},{10,2},{12,4},{14,6},{1,9},{3,11}... | collective-permute-start | bytes 196616 | tf_op jit(solution)/shard_map/ppermute | solution.py:19
  25.4 6.7 %collective-permute-start.2 = (bf16[128,256]{1,0:T(8,128)(2,1)S(1)}, bf16[128,256]{1,0:T(8,128)(2,1)S(1)}, u32[]{:S(2)}, u32[]{:S(2)}) collective-permute-start(bf16[128,256]{1,0:T(8,128)(2,1)S(1)} %get-tuple-element.24), channel_id=1, source_target_pairs={{0,8},{2,10},{4,12},{6,14},{8,0},{10,2},{12,4},{14,6},{1,9},{3,11}... | collective-permute-start | bytes 196616 | tf_op jit(solution)/shard_map/ppermute | solution.py:19
  27.5 5.7 %collective-permute-start.18 = (bf16[128,256]{1,0:T(8,128)(2,1)S(1)}, bf16[128,256]{1,0:T(8,128)(2,1)S(1)}, u32[]{:S(2)}, u32[]{:S(2)}) collective-permute-start(bf16[128,256]{1,0:T(8,128)(2,1)S(1)} %multiply_convert_fusion), channel_id=1, source_target_pairs={{0,2},{2,0},{4,6},{6,4},{8,10},{10,8},{12,14},{14,12},{1,3},{3,1},... | collective-permute-start | bytes 196616 | tf_op jit(solution)/shard_map/ppermute | solution.py:19
  30.1 5.0 %collective-permute-start.13 = (bf16[128,256]{1,0:T(8,128)(2,1)S(1)}, bf16[128,256]{1,0:T(8,128)(2,1)S(1)}, u32[]{:S(2)}, u32[]{:S(2)}) collective-permute-start(bf16[128,256]{1,0:T(8,128)(2,1)S(1)} %multiply_convert_fusion.1), channel_id=1, source_target_pairs={{0,4},{2,6},{4,0},{6,2},{8,12},{10,14},{12,8},{14,10},{1,5},{3,7},... | collective-permute-start | bytes 196616 | tf_op jit(solution)/shard_map/ppermute | solution.py:19
  30.8 5.2 %collective-permute-start.8 = (bf16[128,256]{1,0:T(8,128)(2,1)S(1)}, bf16[128,256]{1,0:T(8,128)(2,1)S(1)}, u32[]{:S(2)}, u32[]{:S(2)}) collective-permute-start(bf16[128,256]{1,0:T(8,128)(2,1)S(1)} %multiply_convert_fusion.2), channel_id=1, source_target_pairs={{0,2},{2,0},{4,6},{6,4},{8,10},{10,8},{12,14},{14,12},{1,3},{3,1},... | collective-permute-start | bytes 196616 | tf_op jit(solution)/shard_map/ppermute | solution.py:19
  32.2 5.1 %collective-permute-start.3 = (bf16[128,256]{1,0:T(8,128)(2,1)S(1)}, bf16[128,256]{1,0:T(8,128)(2,1)S(1)}, u32[]{:S(2)}, u32[]{:S(2)}) collective-permute-start(bf16[128,256]{1,0:T(8,128)(2,1)S(1)} %multiply_convert_fusion.3), channel_id=1, source_target_pairs={{0,4},{2,6},{4,0},{6,2},{8,12},{10,14},{12,8},{14,10},{1,5},{3,7},... | collective-permute-start | bytes 196616 | tf_op jit(solution)/shard_map/ppermute | solution.py:19
  33.2 5.8 %collective-permute-start.19 = (bf16[128,512]{1,0:T(8,128)(2,1)S(1)}, bf16[128,512]{1,0:T(8,128)(2,1)S(1)}, u32[]{:S(2)}, u32[]{:S(2)}) collective-permute-start(bf16[128,512]{1,0:T(8,128)(2,1)S(1)} %pad_maximum_fusion.4), channel_id=1, source_target_pairs={{0,4},{2,6},{4,0},{6,2},{8,12},{10,14},{12,8},{14,10},{1,5},{3,7},... | collective-permute-start | bytes 393224 | tf_op jit(solution)/shard_map/ppermute | solution.py:19
  35.2 5.0 %collective-permute-start.14 = (bf16[128,512]{1,0:T(8,128)(2,1)S(1)}, bf16[128,512]{1,0:T(8,128)(2,1)S(1)}, u32[]{:S(2)}, u32[]{:S(2)}) collective-permute-start(bf16[128,512]{1,0:T(8,128)(2,1)S(1)} %pad_maximum_fusion.3), channel_id=1, source_target_pairs={{0,2},{2,0},{4,6},{6,4},{8,10},{10,8},{12,14},{14,12},{1,3},{3,1},... | collective-permute-start | bytes 393224 | tf_op jit(solution)/shard_map/ppermute | solution.py:19
  36.1 5.0 %collective-permute-start.9 = (bf16[128,512]{1,0:T(8,128)(2,1)S(1)}, bf16[128,512]{1,0:T(8,128)(2,1)S(1)}, u32[]{:S(2)}, u32[]{:S(2)}) collective-permute-start(bf16[128,512]{1,0:T(8,128)(2,1)S(1)} %pad_maximum_fusion.2), channel_id=1, source_target_pairs={{0,4},{2,6},{4,0},{6,2},{8,12},{10,14},{12,8},{14,10},{1,5},{3,7},... | collective-permute-start | bytes 393224 | tf_op jit(solution)/shard_map/ppermute | solution.py:19
  37.3 5.0 %collective-permute-start.4 = (bf16[128,512]{1,0:T(8,128)(2,1)S(1)}, bf16[128,512]{1,0:T(8,128)(2,1)S(1)}, u32[]{:S(2)}, u32[]{:S(2)}) collective-permute-start(bf16[128,512]{1,0:T(8,128)(2,1)S(1)} %pad_maximum_fusion.1), channel_id=1, source_target_pairs={{0,2},{2,0},{4,6},{6,4},{8,10},{10,8},{12,14},{14,12},{1,3},{3,1},... | collective-permute-start | bytes 393224 | tf_op jit(solution)/shard_map/ppermute | solution.py:19
  42.9 1.6 %collective-permute-start.20 = (f32[512,128]{1,0:T(8,128)S(1)}, f32[512,128]{1,0:T(8,128)S(1)}, u32[]{:S(2)}, u32[]{:S(2)}) collective-permute-start(f32[512,128]{1,0:T(8,128)S(1)} %fusion.2.mine_ref), channel_id=1, source_target_pairs={{0,1},{1,0},{2,3},{3,2},{4,5},{5,4},{6,7},{7,6},{8,9},{9,8},{10,11... | collective-permute-start | bytes 786440 | tf_op jit(solution)/shard_map/ppermute | solution.py:19
  45.0 6.8 %collective-permute-start.24 = (f32[72,128]{1,0:T(8,128)S(1)}, f32[72,128]{1,0:T(8,128)S(1)}, u32[]{:S(2)}, u32[]{:S(2)}) collective-permute-start(f32[72,128]{1,0:T(8,128)S(1)} %get-tuple-element.17), channel_id=1, source_target_pairs={{0,10},{1,15},{2,8},{3,13},{4,14},{5,11},{6,12},{7,9},{8,2},{9,7},... | collective-permute-start | bytes 110600 | tf_op jit(solution)/shard_map/ppermute | solution.py:37
  48.4 5.5 %collective-permute-start.23 = (f32[72,128]{1,0:T(8,128)S(1)}, f32[72,128]{1,0:T(8,128)S(1)}, u32[]{:S(2)}, u32[]{:S(2)}) collective-permute-start(f32[72,128]{1,0:T(8,128)S(1)} %get-tuple-element.17), channel_id=1, source_target_pairs={{0,8},{1,13},{2,10},{3,15},{4,12},{5,9},{6,14},{7,11},{8,0},{9,5},... | collective-permute-start | bytes 110600 | tf_op jit(solution)/shard_map/ppermute | solution.py:37
  48.4 5.5 %collective-permute-start.22 = (f32[72,128]{1,0:T(8,128)S(1)}, f32[72,128]{1,0:T(8,128)S(1)}, u32[]{:S(2)}, u32[]{:S(2)}) collective-permute-start(f32[72,128]{1,0:T(8,128)S(1)} %get-tuple-element.17), channel_id=1, source_target_pairs={{0,2},{1,7},{2,0},{3,5},{4,6},{5,3},{6,4},{7,1},{8,10},{9,15},{10,... | collective-permute-start | bytes 110600 | tf_op jit(solution)/shard_map/ppermute | solution.py:37
  49.4 4.4 %collective-permute-start.21 = (f32[72,128]{1,0:T(8,128)S(1)}, f32[72,128]{1,0:T(8,128)S(1)}, u32[]{:S(2)}, u32[]{:S(2)}) collective-permute-start(f32[72,128]{1,0:T(8,128)S(1)} %get-tuple-element.17), channel_id=1, source_target_pairs={{1,5},{3,7},{5,1},{7,3},{9,13},{11,15},{13,9},{15,11},{17,21},{19,... | collective-permute-start | bytes 110600 | tf_op jit(solution)/shard_map/ppermute | solution.py:37
  53.9 1.3 %collective-permute-start.25 = (f32[72,128]{1,0:T(8,128)S(1)}, f32[72,128]{1,0:T(8,128)S(1)}, u32[]{:S(2)}, u32[]{:S(2)}) collective-permute-start(f32[72,128]{1,0:T(8,128)S(1)} %add_add_fusion), channel_id=1, source_target_pairs={{0,1},{1,0},{2,3},{3,2},{4,5},{5,4},{6,7},{7,6},{8,9},{9,8},{10,11... | collective-permute-start | bytes 110600 | tf_op jit(solution)/shard_map/ppermute | solution.py:19
  59.3 6.2 %collective-permute-start.26 = (bf16[2,2,16,1024]{3,2,0,1:T(8,128)(2,1)S(1)}, bf16[2,2,16,1024]{3,2,0,1:T(8,128)(2,1)S(1)}, u32[]{:S(2)}, u32[]{:S(2)}) collective-permute-start(bf16[2,2,16,1024]{3,2,0,1:T(8,128)(2,1)S(1)} %fusion.22), channel_id=1, source_target_pairs={{0,2},{2,0},{4,6},{6,4},{8,10},{10,8},{12,14},{14,12},{1,3},{3,1},... | collective-permute-start | bytes 393224 | tf_op jit(solution)/shard_map/ppermute | solution.py:19
  60.1 7.3 %collective-permute-start.29 = (bf16[2,2,16,1024]{3,2,0,1:T(8,128)(2,1)S(1)}, bf16[2,2,16,1024]{3,2,0,1:T(8,128)(2,1)S(1)}, u32[]{:S(2)}, u32[]{:S(2)}) collective-permute-start(bf16[2,2,16,1024]{3,2,0,1:T(8,128)(2,1)S(1)} %fusion.23), channel_id=1, source_target_pairs={{0,4},{2,6},{4,0},{6,2},{8,12},{10,14},{12,8},{14,10},{1,5},{3,7},... | collective-permute-start | bytes 393224 | tf_op jit(solution)/shard_map/ppermute | solution.py:19
  62.0 6.4 %collective-permute-start.32 = (bf16[2,2,16,1024]{3,2,0,1:T(8,128)(2,1)S(1)}, bf16[2,2,16,1024]{3,2,0,1:T(8,128)(2,1)S(1)}, u32[]{:S(2)}, u32[]{:S(2)}) collective-permute-start(bf16[2,2,16,1024]{3,2,0,1:T(8,128)(2,1)S(1)} %fusion.24), channel_id=1, source_target_pairs={{0,2},{2,0},{4,6},{6,4},{8,10},{10,8},{12,14},{14,12},{1,3},{3,1},... | collective-permute-start | bytes 393224 | tf_op jit(solution)/shard_map/ppermute | solution.py:19
  63.4 6.5 %collective-permute-start.35 = (bf16[2,2,16,1024]{3,2,0,1:T(8,128)(2,1)S(1)}, bf16[2,2,16,1024]{3,2,0,1:T(8,128)(2,1)S(1)}, u32[]{:S(2)}, u32[]{:S(2)}) collective-permute-start(bf16[2,2,16,1024]{3,2,0,1:T(8,128)(2,1)S(1)} %fusion.25), channel_id=1, source_target_pairs={{0,4},{2,6},{4,0},{6,2},{8,12},{10,14},{12,8},{14,10},{1,5},{3,7},... | collective-permute-start | bytes 393224 | tf_op jit(solution)/shard_map/ppermute | solution.py:19
  65.6 5.1 %collective-permute-start.27 = (bf16[2,16,1024]{2,1,0:T(8,128)(2,1)S(1)}, bf16[2,16,1024]{2,1,0:T(8,128)(2,1)S(1)}, u32[]{:S(2)}, u32[]{:S(2)}) collective-permute-start(bf16[2,16,1024]{2,1,0:T(8,128)(2,1)S(1)} %fusion.26), channel_id=1, source_target_pairs={{0,4},{2,6},{4,0},{6,2},{8,12},{10,14},{12,8},{14,10},{1,5},{3,7},... | collective-permute-start | bytes 196616 | tf_op jit(solution)/shard_map/ppermute | solution.py:19
  67.5 6.7 %collective-permute-start.30 = (bf16[2,16,1024]{2,1,0:T(8,128)(2,1)S(1)}, bf16[2,16,1024]{2,1,0:T(8,128)(2,1)S(1)}, u32[]{:S(2)}, u32[]{:S(2)}) collective-permute-start(bf16[2,16,1024]{2,1,0:T(8,128)(2,1)S(1)} %fusion.27), channel_id=1, source_target_pairs={{0,2},{2,0},{4,6},{6,4},{8,10},{10,8},{12,14},{14,12},{1,3},{3,1},... | collective-permute-start | bytes 196616 | tf_op jit(solution)/shard_map/ppermute | solution.py:19
  68.4 6.5 %collective-permute-start.33 = (bf16[2,16,1024]{2,1,0:T(8,128)(2,1)S(1)}, bf16[2,16,1024]{2,1,0:T(8,128)(2,1)S(1)}, u32[]{:S(2)}, u32[]{:S(2)}) collective-permute-start(bf16[2,16,1024]{2,1,0:T(8,128)(2,1)S(1)} %fusion.28), channel_id=1, source_target_pairs={{0,4},{2,6},{4,0},{6,2},{8,12},{10,14},{12,8},{14,10},{1,5},{3,7},... | collective-permute-start | bytes 196616 | tf_op jit(solution)/shard_map/ppermute | solution.py:19
  69.9 7.4 %collective-permute-start.36 = (bf16[2,16,1024]{2,1,0:T(8,128)(2,1)S(1)}, bf16[2,16,1024]{2,1,0:T(8,128)(2,1)S(1)}, u32[]{:S(2)}, u32[]{:S(2)}) collective-permute-start(bf16[2,16,1024]{2,1,0:T(8,128)(2,1)S(1)} %fusion.29), channel_id=1, source_target_pairs={{0,2},{2,0},{4,6},{6,4},{8,10},{10,8},{12,14},{14,12},{1,3},{3,1},... | collective-permute-start | bytes 196616 | tf_op jit(solution)/shard_map/ppermute | solution.py:19
  70.8 7.4 %collective-permute-start.28 = (bf16[16,1024]{1,0:T(8,128)(2,1)S(1)}, bf16[16,1024]{1,0:T(8,128)(2,1)S(1)}, u32[]{:S(2)}, u32[]{:S(2)}) collective-permute-start(bf16[16,1024]{1,0:T(8,128)(2,1)S(1)} %fusion.34), channel_id=1, source_target_pairs={{0,8},{2,10},{4,12},{6,14},{8,0},{10,2},{12,4},{14,6},{1,9},{3,11}... | collective-permute-start | bytes 98312 | tf_op jit(solution)/shard_map/ppermute | solution.py:19
  74.2 5.7 %collective-permute-start.31 = (bf16[16,1024]{1,0:T(8,128)(2,1)S(1)}, bf16[16,1024]{1,0:T(8,128)(2,1)S(1)}, u32[]{:S(2)}, u32[]{:S(2)}) collective-permute-start(bf16[16,1024]{1,0:T(8,128)(2,1)S(1)} %fusion.35), channel_id=1, source_target_pairs={{0,8},{2,10},{4,12},{6,14},{8,0},{10,2},{12,4},{14,6},{1,9},{3,11}... | collective-permute-start | bytes 98312 | tf_op jit(solution)/shard_map/ppermute | solution.py:19
  75.0 5.6 %collective-permute-start.34 = (bf16[16,1024]{1,0:T(8,128)(2,1)S(1)}, bf16[16,1024]{1,0:T(8,128)(2,1)S(1)}, u32[]{:S(2)}, u32[]{:S(2)}) collective-permute-start(bf16[16,1024]{1,0:T(8,128)(2,1)S(1)} %fusion.36), channel_id=1, source_target_pairs={{0,8},{2,10},{4,12},{6,14},{8,0},{10,2},{12,4},{14,6},{1,9},{3,11}... | collective-permute-start | bytes 98312 | tf_op jit(solution)/shard_map/ppermute | solution.py:19
  77.4 5.0 %collective-permute-start.37 = (bf16[16,1024]{1,0:T(8,128)(2,1)S(1)}, bf16[16,1024]{1,0:T(8,128)(2,1)S(1)}, u32[]{:S(2)}, u32[]{:S(2)}) collective-permute-start(bf16[16,1024]{1,0:T(8,128)(2,1)S(1)} %fusion.37), channel_id=1, source_target_pairs={{0,8},{2,10},{4,12},{6,14},{8,0},{10,2},{12,4},{14,6},{1,9},{3,11}... | collective-permute-start | bytes 98312 | tf_op jit(solution)/shard_map/ppermute | solution.py:19

commit v30 on v25

--- a/solution.py
+++ b/solution.py
@@ -84,8 +84,9 @@
 def orders_of(axis):
     bits = list(range((lax.axis_size(axis) - 1).bit_length()))
     if len(bits) < 3:
-        return [bits, bits]
-    return [bits, [bits[1], bits[0]] + bits[2:]]
+        return [bits] * 4
+    heads = [(0, 1, 2), (1, 0, 2), (0, 2, 1), (1, 2, 0)]
+    return [list(head) + bits[3:] for head in heads]
 
 
 def fetch_tiles(slab_ref, begin, buffer, arrived):
@@ -323,7 +324,7 @@
     packed, sketch = make_gram(partial_sketch, other_sketch, total_cols)
     basis, *products = make_basis(row_sum(packed), sketch, activations, root_rows, CHUNKS)
     pieces = [
-        scatter_sum(product, "row", orders[c % 2]) / total_rows
+        scatter_sum(product, "row", orders[c % 4]) / total_rows
         for c, product in enumerate(products)
     ]
     return (basis, jnp.concatenate(pieces, axis=1))

time: 81.8 us -> 85.4 us (1.044)
  waiting for transfers between devices: 22.3 us -> 29.6 us
  starting transfers between devices: 44.5 us -> 40.9 us
    ppermute x34, waiting for transfers between devices: 19.6 us -> 24.9 us  [swap(): return lax.ppermute(value, axis, [(i, i ^ distance) for i in range(size)])]
    ppermute x34, starting transfers between devices: 39.4 us -> 35.8 us  [swap(): return lax.ppermute(value, axis, [(i, i ^ distance) for i in range(size)])]
    ppermute x4, waiting for transfers between devices: 2.67 us -> 4.63 us  [row_sum(): terms.append(lax.ppermute(value, ('row', 'col'), pairs))]
  transfers between devices with their start and end apart: 38 -> 38, of which waited for: 19 -> 21; matrix products, arithmetic and copies ran while one was open for 3% -> 3% of each run, Pallas kernels for 2% -> 2%
where the time goes in v30:
time: 85.4 us; the launch traced here: 85.2 us
  starting transfers between devices  40.9 us (48%)
  waiting for transfers between devices  29.6 us (35%)
  Pallas kernels  8.68 us (10%)
  other arithmetic  2.13 us (2%)
  matrix products  1.77 us (2%)
  between operations  1.14 us (1%)
  local copies, waits for them, and re-layouts  0.98 us (1%)
    ppermute x34, starting transfers between devices, swap(): return lax.ppermute(value, axis, [(i, i ^ distance) for i in range(size)])  35.8 us
    ppermute x34, waiting for transfers between devices, swap(): return lax.ppermute(value, axis, [(i, i ^ distance) for i in range(size)])  24.9 us
    ppermute x4, starting transfers between devices, row_sum(): terms.append(lax.ppermute(value, ('row', 'col'), pairs))  5.12 us
    ppermute x4, waiting for transfers between devices, row_sum(): terms.append(lax.ppermute(value, ('row', 'col'), pairs))  4.63 us
    pallas_call x1, Pallas kernels, make_basis(): pl.pallas_call(functools.partial(basis_kernel, root_rows), out_shape=[jax...  4.1 us
    pallas_call x2, Pallas kernels, first_product(): pl.pallas_call(functools.partial(sketch_kernel, begin), out_shape=[jax.Sh...  4.07 us
    dot_general x4, matrix products, per_device(): lax.dot_general(activations[:, span], shared, (((1,), (1,)), ((), ())), p...  1.77 us
  transfers between devices with their start and end apart: 38, of which 21 were waited for; matrix products, arithmetic and copies ran while one was open for 3% of the time, Pallas kernels for 2%

profile of v30, /device:TPU:0, one launch (start us, length us, event | category | flops | bytes accessed | tf_op | source)
XLA Modules:
  0.0 85.2 jit_solution(4578440749359528190)
XLA Ops:
  0.6 0.9 %copy-done = bf16[512,128]{1,0:T(8,128)(2,1)S(1)} copy-done((bf16[512,128]{1,0:T(8,128)(2,1)S(1)}, bf16[512,128]{1,0:T(8,128)(2,1)}, u32[]{:S(2)}) %copy-start) | copy-done | bytes 131096
  1.5 2.1 %first_product.2 = (f32[128,1024]{1,0:T(8,128)S(1)}, f32[128,1024]{1,0:T(8,128)S(1)}) custom-call(bf16[512,128]{1,0:T(8,128)(2,1)S(1)} %copy-done, bf16[512,4096]{1,0:T(8,128)(2,1)} %slab_ref.5), custom_call_target="tpu_custom_call" | custom-call | flops 268435456 | bytes 2097152 | tf_op jit(solution)/shard_map/first_product/pallas_call | solution.py:118
  3.6 3.0 %collective-permute-start = (bf16[128,512]{1,0:T(8,128)(2,1)S(1)}, bf16[128,512]{1,0:T(8,128)(2,1)S(1)}, u32[]{:S(2)}, u32[]{:S(2)}) collective-permute-start(bf16[128,512]{1,0:T(8,128)(2,1)S(1)} %select_convert_fusion.7), channel_id=1, source_target_pairs={{0,2},{2,0},{4,6},{6,4},{8,10},{10,8},{12,14},{14,12},{1,3},{3,1},... | collective-permute-start | bytes 393224 | tf_op jit(solution)/shard_map/ppermute | solution.py:18
  6.7 1.6 %collective-permute-start.5 = (bf16[128,512]{1,0:T(8,128)(2,1)S(1)}, bf16[128,512]{1,0:T(8,128)(2,1)S(1)}, u32[]{:S(2)}, u32[]{:S(2)}) collective-permute-start(bf16[128,512]{1,0:T(8,128)(2,1)S(1)} %select_convert_fusion.6), channel_id=1, source_target_pairs={{0,4},{2,6},{4,0},{6,2},{8,12},{10,14},{12,8},{14,10},{1,5},{3,7},... | collective-permute-start | bytes 393224 | tf_op jit(solution)/shard_map/ppermute | solution.py:18
  8.3 2.0 %first_product.3 = (f32[128,1024]{1,0:T(8,128)S(1)}, f32[128,1024]{1,0:T(8,128)S(1)}) custom-call(bf16[512,128]{1,0:T(8,128)(2,1)S(1)} %copy-done.1, bf16[512,4096]{1,0:T(8,128)(2,1)} %slab_ref.5), custom_call_target="tpu_custom_call" | custom-call | flops 268435456 | bytes 2097152 | tf_op jit(solution)/shard_map/first_product/pallas_call | solution.py:118
  10.4 0.6 collective-permute-start.10
  11.2 2.1 %collective-permute-start.1 = (bf16[128,256]{1,0:T(8,128)(2,1)S(1)}, bf16[128,256]{1,0:T(8,128)(2,1)S(1)}, u32[]{:S(2)}, u32[]{:S(2)}) collective-permute-start(bf16[128,256]{1,0:T(8,128)(2,1)S(1)} %select_convert_fusion.15), channel_id=1, source_target_pairs={{0,4},{2,6},{4,0},{6,2},{8,12},{10,14},{12,8},{14,10},{1,5},{3,7},... | collective-permute-start | bytes 196616 | tf_op jit(solution)/shard_map/ppermute | solution.py:18
  13.3 1.6 %collective-permute-start.6 = (bf16[128,256]{1,0:T(8,128)(2,1)S(1)}, bf16[128,256]{1,0:T(8,128)(2,1)S(1)}, u32[]{:S(2)}, u32[]{:S(2)}) collective-permute-start(bf16[128,256]{1,0:T(8,128)(2,1)S(1)} %select_convert_fusion.14), channel_id=1, source_target_pairs={{0,2},{2,0},{4,6},{6,4},{8,10},{10,8},{12,14},{14,12},{1,3},{3,1},... | collective-permute-start | bytes 196616 | tf_op jit(solution)/shard_map/ppermute | solution.py:18
  14.9 1.2 %collective-permute-done.10 = bf16[128,512]{1,0:T(8,128)(2,1)S(1)} collective-permute-done((bf16[128,512]{1,0:T(8,128)(2,1)S(1)}, bf16[128,512]{1,0:T(8,128)(2,1)S(1)}, u32[]{:S(2)}, u32[]{:S(2)}) %collective-permute-start.10) | collective-permute-done | bytes 131104 | tf_op jit(solution)/shard_map/ppermute | solution.py:18
  16.8 1.7 %collective-permute-start.16 = (bf16[128,256]{1,0:T(8,128)(2,1)S(1)}, bf16[128,256]{1,0:T(8,128)(2,1)S(1)}, u32[]{:S(2)}, u32[]{:S(2)}) collective-permute-start(bf16[128,256]{1,0:T(8,128)(2,1)S(1)} %select_convert_fusion.12), channel_id=1, source_target_pairs={{0,2},{2,0},{4,6},{6,4},{8,10},{10,8},{12,14},{14,12},{1,3},{3,1},... | collective-permute-start | bytes 196616 | tf_op jit(solution)/shard_map/ppermute | solution.py:18
  18.5 2.7 %collective-permute-start.2 = (bf16[128,256]{1,0:T(8,128)(2,1)S(1)}, bf16[128,256]{1,0:T(8,128)(2,1)S(1)}, u32[]{:S(2)}, u32[]{:S(2)}) collective-permute-start(bf16[128,256]{1,0:T(8,128)(2,1)S(1)} %fusion.42), channel_id=1, source_target_pairs={{0,8},{2,10},{4,12},{6,14},{8,0},{10,2},{12,4},{14,6},{1,9},{3,11}... | collective-permute-start | bytes 196616 | tf_op jit(solution)/shard_map/ppermute | solution.py:18
  21.7 2.7 %collective-permute-start.12 = (bf16[128,256]{1,0:T(8,128)(2,1)S(1)}, bf16[128,256]{1,0:T(8,128)(2,1)S(1)}, u32[]{:S(2)}, u32[]{:S(2)}) collective-permute-start(bf16[128,256]{1,0:T(8,128)(2,1)S(1)} %fusion.44), channel_id=1, source_target_pairs={{0,8},{2,10},{4,12},{6,14},{8,0},{10,2},{12,4},{14,6},{1,9},{3,11}... | collective-permute-start | bytes 196616 | tf_op jit(solution)/shard_map/ppermute | solution.py:18
  24.7 3.0 %collective-permute-done.2 = bf16[128,256]{1,0:T(8,128)(2,1)S(1)} collective-permute-done((bf16[128,256]{1,0:T(8,128)(2,1)S(1)}, bf16[128,256]{1,0:T(8,128)(2,1)S(1)}, u32[]{:S(2)}, u32[]{:S(2)}) %collective-permute-start.2) | collective-permute-done | bytes 65568 | tf_op jit(solution)/shard_map/ppermute | solution.py:18
  27.9 2.0 %collective-permute-done.7 = bf16[128,256]{1,0:T(8,128)(2,1)S(1)} collective-permute-done((bf16[128,256]{1,0:T(8,128)(2,1)S(1)}, bf16[128,256]{1,0:T(8,128)(2,1)S(1)}, u32[]{:S(2)}, u32[]{:S(2)}) %collective-permute-start.7) | collective-permute-done | bytes 65568 | tf_op jit(solution)/shard_map/ppermute | solution.py:18
  30.7 0.7 collective-permute-done.17
  31.4 1.1 %collective-permute-start.18 = (bf16[128,256]{1,0:T(8,128)(2,1)S(1)}, bf16[128,256]{1,0:T(8,128)(2,1)S(1)}, u32[]{:S(2)}, u32[]{:S(2)}) collective-permute-start(bf16[128,256]{1,0:T(8,128)(2,1)S(1)} %multiply_convert_fusion), channel_id=1, source_target_pairs={{0,2},{2,0},{4,6},{6,4},{8,10},{10,8},{12,14},{14,12},{1,3},{3,1},... | collective-permute-start | bytes 196616 | tf_op jit(solution)/shard_map/ppermute | solution.py:18
  32.7 0.9 %collective-permute-start.4 = (bf16[128,512]{1,0:T(8,128)(2,1)S(1)}, bf16[128,512]{1,0:T(8,128)(2,1)S(1)}, u32[]{:S(2)}, u32[]{:S(2)}) collective-permute-start(bf16[128,512]{1,0:T(8,128)(2,1)S(1)} %pad_maximum_fusion.1), channel_id=1, source_target_pairs={{0,2},{2,0},{4,6},{6,4},{8,10},{10,8},{12,14},{14,12},{1,3},{3,1},... | collective-permute-start | bytes 393224 | tf_op jit(solution)/shard_map/ppermute | solution.py:18
  33.6 1.2 %collective-permute-done.8 = bf16[128,256]{1,0:T(8,128)(2,1)S(1)} collective-permute-done((bf16[128,256]{1,0:T(8,128)(2,1)S(1)}, bf16[128,256]{1,0:T(8,128)(2,1)S(1)}, u32[]{:S(2)}, u32[]{:S(2)}) %collective-permute-start.8) | collective-permute-done | bytes 65568 | tf_op jit(solution)/shard_map/ppermute | solution.py:18
  35.5 1.6 %collective-permute-start.14 = (bf16[128,512]{1,0:T(8,128)(2,1)S(1)}, bf16[128,512]{1,0:T(8,128)(2,1)S(1)}, u32[]{:S(2)}, u32[]{:S(2)}) collective-permute-start(bf16[128,512]{1,0:T(8,128)(2,1)S(1)} %pad_maximum_fusion.3), channel_id=1, source_target_pairs={{0,2},{2,0},{4,6},{6,4},{8,10},{10,8},{12,14},{14,12},{1,3},{3,1},... | collective-permute-start | bytes 393224 | tf_op jit(solution)/shard_map/ppermute | solution.py:18
  37.2 0.7 collective-permute-start.19
  37.8 1.9 %collective-permute-done.9 = bf16[128,512]{1,0:T(8,128)(2,1)S(1)} collective-permute-done((bf16[128,512]{1,0:T(8,128)(2,1)S(1)}, bf16[128,512]{1,0:T(8,128)(2,1)S(1)}, u32[]{:S(2)}, u32[]{:S(2)}) %collective-permute-start.9) | collective-permute-done | bytes 131104 | tf_op jit(solution)/shard_map/ppermute | solution.py:18
  41.1 1.2 %collective-permute-done.19 = bf16[128,512]{1,0:T(8,128)(2,1)S(1)} collective-permute-done((bf16[128,512]{1,0:T(8,128)(2,1)S(1)}, bf16[128,512]{1,0:T(8,128)(2,1)S(1)}, u32[]{:S(2)}, u32[]{:S(2)}) %collective-permute-start.19) | collective-permute-done | bytes 131104 | tf_op jit(solution)/shard_map/ppermute | solution.py:18
  43.3 1.5 %collective-permute-done.20.other_ref = f32[512,128]{1,0:T(8,128)S(1)} collective-permute-done((f32[512,128]{1,0:T(8,128)S(1)}, f32[512,128]{1,0:T(8,128)S(1)}, u32[]{:S(2)}, u32[]{:S(2)}) %collective-permute-start.20) | collective-permute-done | bytes 262176 | tf_op jit(solution)/shard_map/ppermute | solution.py:18
  45.3 0.7 collective-permute-start.21
  46.0 0.5 collective-permute-start.22
  46.6 1.7 %collective-permute-start.23 = (f32[72,128]{1,0:T(8,128)S(1)}, f32[72,128]{1,0:T(8,128)S(1)}, u32[]{:S(2)}, u32[]{:S(2)}) collective-permute-start(f32[72,128]{1,0:T(8,128)S(1)} %get-tuple-element.17), channel_id=1, source_target_pairs={{0,8},{1,13},{2,10},{3,15},{4,12},{5,9},{6,14},{7,11},{8,0},{9,5},... | collective-permute-start | bytes 110600 | tf_op jit(solution)/shard_map/ppermute | solution.py:36
  48.3 2.2 %collective-permute-start.24 = (f32[72,128]{1,0:T(8,128)S(1)}, f32[72,128]{1,0:T(8,128)S(1)}, u32[]{:S(2)}, u32[]{:S(2)}) collective-permute-start(f32[72,128]{1,0:T(8,128)S(1)} %get-tuple-element.17), channel_id=1, source_target_pairs={{0,10},{1,15},{2,8},{3,13},{4,14},{5,11},{6,12},{7,9},{8,2},{9,7},... | collective-permute-start | bytes 110600 | tf_op jit(solution)/shard_map/ppermute | solution.py:36
  50.5 1.0 %collective-permute-done.23 = f32[72,128]{1,0:T(8,128)S(1)} collective-permute-done((f32[72,128]{1,0:T(8,128)S(1)}, f32[72,128]{1,0:T(8,128)S(1)}, u32[]{:S(2)}, u32[]{:S(2)}) %collective-permute-start.23) | collective-permute-done | bytes 36896 | tf_op jit(solution)/shard_map/ppermute | solution.py:36
  51.5 3.7 %collective-permute-done.24 = f32[72,128]{1,0:T(8,128)S(1)} collective-permute-done((f32[72,128]{1,0:T(8,128)S(1)}, f32[72,128]{1,0:T(8,128)S(1)}, u32[]{:S(2)}, u32[]{:S(2)}) %collective-permute-start.24) | collective-permute-done | bytes 36896 | tf_op jit(solution)/shard_map/ppermute | solution.py:36
  55.1 1.2 %collective-permute-start.25 = (f32[72,128]{1,0:T(8,128)S(1)}, f32[72,128]{1,0:T(8,128)S(1)}, u32[]{:S(2)}, u32[]{:S(2)}) collective-permute-start(f32[72,128]{1,0:T(8,128)S(1)} %add_add_fusion), channel_id=1, source_target_pairs={{0,1},{1,0},{2,3},{3,2},{4,5},{5,4},{6,7},{7,6},{8,9},{9,8},{10,11... | collective-permute-start | bytes 110600 | tf_op jit(solution)/shard_map/ppermute | solution.py:18
  56.3 0.9 %collective-permute-done.25 = f32[72,128]{1,0:T(8,128)S(1)} collective-permute-done((f32[72,128]{1,0:T(8,128)S(1)}, f32[72,128]{1,0:T(8,128)S(1)}, u32[]{:S(2)}, u32[]{:S(2)}) %collective-permute-start.25) | collective-permute-done | bytes 36896 | tf_op jit(solution)/shard_map/ppermute | solution.py:18
  57.2 4.1 %make_basis.1 = (f32[512,128]{1,0:T(8,128)}, f32[128,1024]{1,0:T(8,128)S(1)}, f32[128,1024]{1,0:T(8,128)S(1)}, f32[128,1024]{1,0:T(8,128)S(1)}, f32[128,1024]{1,0:T(8,128)S(1)}) custom-call(f32[72,128]{1,0:T(8,128)S(1)} %add.116.gram_ref, f32[128,512]{1,0:T(8,128)S(1)} %get-tuple-element.18.sketch_ref, bf16[512,4096]{1,0:T(8,128)(2,1)} %slab_ref.5), custom_call_target="tpu_custom_call" | custom-call | tf_op jit(solution)/shard_map/make_basis/pallas_call | solution.py:280
  61.3 1.1 %collective-permute-start.26 = (bf16[2,2,16,1024]{3,2,1,0:T(8,128)(2,1)S(1)}, bf16[2,2,16,1024]{3,2,1,0:T(8,128)(2,1)S(1)}, u32[]{:S(2)}, u32[]{:S(2)}) collective-permute-start(bf16[2,2,16,1024]{3,2,1,0:T(8,128)(2,1)S(1)} %fusion.22), channel_id=1, source_target_pairs={{0,2},{2,0},{4,6},{6,4},{8,10},{10,8},{12,14},{14,12},{1,3},{3,1},... | collective-permute-start | bytes 393224 | tf_op jit(solution)/shard_map/ppermute | solution.py:18
  62.6 1.1 %collective-permute-start.32 = (bf16[2,2,16,1024]{3,2,1,0:T(8,128)(2,1)S(1)}, bf16[2,2,16,1024]{3,2,1,0:T(8,128)(2,1)S(1)}, u32[]{:S(2)}, u32[]{:S(2)}) collective-permute-start(bf16[2,2,16,1024]{3,2,1,0:T(8,128)(2,1)S(1)} %fusion.24), channel_id=1, source_target_pairs={{0,2},{2,0},{4,6},{6,4},{8,10},{10,8},{12,14},{14,12},{1,3},{3,1},... | collective-permute-start | bytes 393224 | tf_op jit(solution)/shard_map/ppermute | solution.py:18
  63.7 2.1 %collective-permute-start.35 = (bf16[2,2,16,1024]{3,2,0,1:T(8,128)(2,1)S(1)}, bf16[2,2,16,1024]{3,2,0,1:T(8,128)(2,1)S(1)}, u32[]{:S(2)}, u32[]{:S(2)}) collective-permute-start(bf16[2,2,16,1024]{3,2,0,1:T(8,128)(2,1)S(1)} %fusion.25), channel_id=1, source_target_pairs={{0,4},{2,6},{4,0},{6,2},{8,12},{10,14},{12,8},{14,10},{1,5},{3,7},... | collective-permute-start | bytes 393224 | tf_op jit(solution)/shard_map/ppermute | solution.py:18
  65.8 1.9 %collective-permute-done.26 = bf16[2,2,16,1024]{3,2,1,0:T(8,128)(2,1)S(1)} collective-permute-done((bf16[2,2,16,1024]{3,2,1,0:T(8,128)(2,1)S(1)}, bf16[2,2,16,1024]{3,2,1,0:T(8,128)(2,1)S(1)}, u32[]{:S(2)}, u32[]{:S(2)}) %collective-permute-start.26) | collective-permute-done | bytes 131104 | tf_op jit(solution)/shard_map/ppermute | solution.py:18
  67.8 1.0 %collective-permute-done.29 = bf16[2,2,16,1024]{3,2,0,1:T(8,128)(2,1)S(1)} collective-permute-done((bf16[2,2,16,1024]{3,2,0,1:T(8,128)(2,1)S(1)}, bf16[2,2,16,1024]{3,2,0,1:T(8,128)(2,1)S(1)}, u32[]{:S(2)}, u32[]{:S(2)}) %collective-permute-start.29) | collective-permute-done | bytes 131104 | tf_op jit(solution)/shard_map/ppermute | solution.py:18
  68.9 1.1 %collective-permute-start.30 = (bf16[2,16,1024]{2,1,0:T(8,128)(2,1)S(1)}, bf16[2,16,1024]{2,1,0:T(8,128)(2,1)S(1)}, u32[]{:S(2)}, u32[]{:S(2)}) collective-permute-start(bf16[2,16,1024]{2,1,0:T(8,128)(2,1)S(1)} %fusion.31), channel_id=1, source_target_pairs={{0,2},{2,0},{4,6},{6,4},{8,10},{10,8},{12,14},{14,12},{1,3},{3,1},... | collective-permute-start | bytes 196616 | tf_op jit(solution)/shard_map/ppermute | solution.py:18
  70.1 1.8 %collective-permute-start.33 = (bf16[2,16,1024]{2,1,0:T(8,128)(2,1)S(1)}, bf16[2,16,1024]{2,1,0:T(8,128)(2,1)S(1)}, u32[]{:S(2)}, u32[]{:S(2)}) collective-permute-start(bf16[2,16,1024]{2,1,0:T(8,128)(2,1)S(1)} %fusion.32), channel_id=1, source_target_pairs={{0,8},{2,10},{4,12},{6,14},{8,0},{10,2},{12,4},{14,6},{1,9},{3,11}... | collective-permute-start | bytes 196616 | tf_op jit(solution)/shard_map/ppermute | solution.py:18
  72.0 1.3 %collective-permute-start.36 = (bf16[2,16,1024]{2,1,0:T(8,128)(2,1)S(1)}, bf16[2,16,1024]{2,1,0:T(8,128)(2,1)S(1)}, u32[]{:S(2)}, u32[]{:S(2)}) collective-permute-start(bf16[2,16,1024]{2,1,0:T(8,128)(2,1)S(1)} %fusion.33), channel_id=1, source_target_pairs={{0,8},{2,10},{4,12},{6,14},{8,0},{10,2},{12,4},{14,6},{1,9},{3,11}... | collective-permute-start | bytes 196616 | tf_op jit(solution)/shard_map/ppermute | solution.py:18
  73.3 1.8 %collective-permute-start.28 = (bf16[16,1024]{1,0:T(8,128)(2,1)S(1)}, bf16[16,1024]{1,0:T(8,128)(2,1)S(1)}, u32[]{:S(2)}, u32[]{:S(2)}) collective-permute-start(bf16[16,1024]{1,0:T(8,128)(2,1)S(1)} %fusion.38), channel_id=1, source_target_pairs={{0,8},{2,10},{4,12},{6,14},{8,0},{10,2},{12,4},{14,6},{1,9},{3,11}... | collective-permute-start | bytes 98312 | tf_op jit(solution)/shard_map/ppermute | solution.py:18
  75.1 1.3 %collective-permute-start.31 = (bf16[16,1024]{1,0:T(8,128)(2,1)S(1)}, bf16[16,1024]{1,0:T(8,128)(2,1)S(1)}, u32[]{:S(2)}, u32[]{:S(2)}) collective-permute-start(bf16[16,1024]{1,0:T(8,128)(2,1)S(1)} %fusion.39), channel_id=1, source_target_pairs={{0,8},{2,10},{4,12},{6,14},{8,0},{10,2},{12,4},{14,6},{1,9},{3,11}... | collective-permute-start | bytes 98312 | tf_op jit(solution)/shard_map/ppermute | solution.py:18
  76.4 2.9 %collective-permute-done.33 = bf16[2,16,1024]{2,1,0:T(8,128)(2,1)S(1)} collective-permute-done((bf16[2,16,1024]{2,1,0:T(8,128)(2,1)S(1)}, bf16[2,16,1024]{2,1,0:T(8,128)(2,1)S(1)}, u32[]{:S(2)}, u32[]{:S(2)}) %collective-permute-start.33) | collective-permute-done | bytes 65568 | tf_op jit(solution)/shard_map/ppermute | solution.py:18
  79.4 1.1 %collective-permute-done.36 = bf16[2,16,1024]{2,1,0:T(8,128)(2,1)S(1)} collective-permute-done((bf16[2,16,1024]{2,1,0:T(8,128)(2,1)S(1)}, bf16[2,16,1024]{2,1,0:T(8,128)(2,1)S(1)}, u32[]{:S(2)}, u32[]{:S(2)}) %collective-permute-start.36) | collective-permute-done | bytes 65568 | tf_op jit(solution)/shard_map/ppermute | solution.py:18
  80.5 0.7 collective-permute-start.37
  81.2 2.0 %collective-permute-done.34 = bf16[16,1024]{1,0:T(8,128)(2,1)S(1)} collective-permute-done((bf16[16,1024]{1,0:T(8,128)(2,1)S(1)}, bf16[16,1024]{1,0:T(8,128)(2,1)S(1)}, u32[]{:S(2)}, u32[]{:S(2)}) %collective-permute-start.34) | collective-permute-done | bytes 32800 | tf_op jit(solution)/shard_map/ppermute | solution.py:18
  83.3 1.2 %collective-permute-done.37 = bf16[16,1024]{1,0:T(8,128)(2,1)S(1)} collective-permute-done((bf16[16,1024]{1,0:T(8,128)(2,1)S(1)}, bf16[16,1024]{1,0:T(8,128)(2,1)S(1)}, u32[]{:S(2)}, u32[]{:S(2)}) %collective-permute-start.37) | collective-permute-done | bytes 32800 | tf_op jit(solution)/shard_map/ppermute | solution.py:18
  84.5 0.7 pad_maximum_fusion
  (103 shorter events, 7.5 us)
Async XLA Ops:
  0.6 0.9 %copy-start = (bf16[512,128]{1,0:T(8,128)(2,1)S(1)}, bf16[512,128]{1,0:T(8,128)(2,1)}, u32[]{:S(2)}) copy-start(bf16[512,128]{1,0:T(8,128)(2,1)} %start_ref.3) | copy-start | bytes 393220
  1.5 6.8 %copy-start.1 = (bf16[512,128]{1,0:T(8,128)(2,1)S(1)}, bf16[512,128]{1,0:T(8,128)(2,1)}, u32[]{:S(2)}) copy-start(bf16[512,128]{1,0:T(8,128)(2,1)} %start_ref.3) | copy-start | bytes 393220
  3.6 7.5 %collective-permute-start = (bf16[128,512]{1,0:T(8,128)(2,1)S(1)}, bf16[128,512]{1,0:T(8,128)(2,1)S(1)}, u32[]{:S(2)}, u32[]{:S(2)}) collective-permute-start(bf16[128,512]{1,0:T(8,128)(2,1)S(1)} %select_convert_fusion.7), channel_id=1, source_target_pairs={{0,2},{2,0},{4,6},{6,4},{8,10},{10,8},{12,14},{14,12},{1,3},{3,1},... | collective-permute-start | bytes 393224 | tf_op jit(solution)/shard_map/ppermute | solution.py:18
  6.7 6.6 %collective-permute-start.5 = (bf16[128,512]{1,0:T(8,128)(2,1)S(1)}, bf16[128,512]{1,0:T(8,128)(2,1)S(1)}, u32[]{:S(2)}, u32[]{:S(2)}) collective-permute-start(bf16[128,512]{1,0:T(8,128)(2,1)S(1)} %select_convert_fusion.6), channel_id=1, source_target_pairs={{0,4},{2,6},{4,0},{6,2},{8,12},{10,14},{12,8},{14,10},{1,5},{3,7},... | collective-permute-start | bytes 393224 | tf_op jit(solution)/shard_map/ppermute | solution.py:18
  10.4 5.7 %collective-permute-start.10 = (bf16[128,512]{1,0:T(8,128)(2,1)S(1)}, bf16[128,512]{1,0:T(8,128)(2,1)S(1)}, u32[]{:S(2)}, u32[]{:S(2)}) collective-permute-start(bf16[128,512]{1,0:T(8,128)(2,1)S(1)} %select_convert_fusion.5), channel_id=1, source_target_pairs={{0,2},{2,0},{4,6},{6,4},{8,10},{10,8},{12,14},{14,12},{1,3},{3,1},... | collective-permute-start | bytes 393224 | tf_op jit(solution)/shard_map/ppermute | solution.py:18
  11.0 5.7 %collective-permute-start.15 = (bf16[128,512]{1,0:T(8,128)(2,1)S(1)}, bf16[128,512]{1,0:T(8,128)(2,1)S(1)}, u32[]{:S(2)}, u32[]{:S(2)}) collective-permute-start(bf16[128,512]{1,0:T(8,128)(2,1)S(1)} %select_convert_fusion.4), channel_id=1, source_target_pairs={{0,4},{2,6},{4,0},{6,2},{8,12},{10,14},{12,8},{14,10},{1,5},{3,7},... | collective-permute-start | bytes 393224 | tf_op jit(solution)/shard_map/ppermute | solution.py:18
  11.2 7.3 %collective-permute-start.1 = (bf16[128,256]{1,0:T(8,128)(2,1)S(1)}, bf16[128,256]{1,0:T(8,128)(2,1)S(1)}, u32[]{:S(2)}, u32[]{:S(2)}) collective-permute-start(bf16[128,256]{1,0:T(8,128)(2,1)S(1)} %select_convert_fusion.15), channel_id=1, source_target_pairs={{0,4},{2,6},{4,0},{6,2},{8,12},{10,14},{12,8},{14,10},{1,5},{3,7},... | collective-permute-start | bytes 196616 | tf_op jit(solution)/shard_map/ppermute | solution.py:18
  13.3 26.5 %copy-start.2 = (bf16[512,4096]{1,0:T(8,128)(2,1)S(1)}, bf16[512,4096]{1,0:T(8,128)(2,1)}, u32[]{:S(2)}) copy-start(bf16[512,4096]{1,0:T(8,128)(2,1)} %slab_ref.5) | copy-start | bytes 12582916
  13.3 7.9 %collective-permute-start.6 = (bf16[128,256]{1,0:T(8,128)(2,1)S(1)}, bf16[128,256]{1,0:T(8,128)(2,1)S(1)}, u32[]{:S(2)}, u32[]{:S(2)}) collective-permute-start(bf16[128,256]{1,0:T(8,128)(2,1)S(1)} %select_convert_fusion.14), channel_id=1, source_target_pairs={{0,2},{2,0},{4,6},{6,4},{8,10},{10,8},{12,14},{14,12},{1,3},{3,1},... | collective-permute-start | bytes 196616 | tf_op jit(solution)/shard_map/ppermute | solution.py:18
  16.2 5.4 %collective-permute-start.11 = (bf16[128,256]{1,0:T(8,128)(2,1)S(1)}, bf16[128,256]{1,0:T(8,128)(2,1)S(1)}, u32[]{:S(2)}, u32[]{:S(2)}) collective-permute-start(bf16[128,256]{1,0:T(8,128)(2,1)S(1)} %select_convert_fusion.13), channel_id=1, source_target_pairs={{0,4},{2,6},{4,0},{6,2},{8,12},{10,14},{12,8},{14,10},{1,5},{3,7},... | collective-permute-start | bytes 196616 | tf_op jit(solution)/shard_map/ppermute | solution.py:18
  16.8 7.5 %collective-permute-start.16 = (bf16[128,256]{1,0:T(8,128)(2,1)S(1)}, bf16[128,256]{1,0:T(8,128)(2,1)S(1)}, u32[]{:S(2)}, u32[]{:S(2)}) collective-permute-start(bf16[128,256]{1,0:T(8,128)(2,1)S(1)} %select_convert_fusion.12), channel_id=1, source_target_pairs={{0,2},{2,0},{4,6},{6,4},{8,10},{10,8},{12,14},{14,12},{1,3},{3,1},... | collective-permute-start | bytes 196616 | tf_op jit(solution)/shard_map/ppermute | solution.py:18
  18.5 9.2 %collective-permute-start.2 = (bf16[128,256]{1,0:T(8,128)(2,1)S(1)}, bf16[128,256]{1,0:T(8,128)(2,1)S(1)}, u32[]{:S(2)}, u32[]{:S(2)}) collective-permute-start(bf16[128,256]{1,0:T(8,128)(2,1)S(1)} %fusion.42), channel_id=1, source_target_pairs={{0,8},{2,10},{4,12},{6,14},{8,0},{10,2},{12,4},{14,6},{1,9},{3,11}... | collective-permute-start | bytes 196616 | tf_op jit(solution)/shard_map/ppermute | solution.py:18
  21.2 8.6 %collective-permute-start.7 = (bf16[128,256]{1,0:T(8,128)(2,1)S(1)}, bf16[128,256]{1,0:T(8,128)(2,1)S(1)}, u32[]{:S(2)}, u32[]{:S(2)}) collective-permute-start(bf16[128,256]{1,0:T(8,128)(2,1)S(1)} %fusion.43), channel_id=1, source_target_pairs={{0,8},{2,10},{4,12},{6,14},{8,0},{10,2},{12,4},{14,6},{1,9},{3,11}... | collective-permute-start | bytes 196616 | tf_op jit(solution)/shard_map/ppermute | solution.py:18
  21.7 8.9 %collective-permute-start.12 = (bf16[128,256]{1,0:T(8,128)(2,1)S(1)}, bf16[128,256]{1,0:T(8,128)(2,1)S(1)}, u32[]{:S(2)}, u32[]{:S(2)}) collective-permute-start(bf16[128,256]{1,0:T(8,128)(2,1)S(1)} %fusion.44), channel_id=1, source_target_pairs={{0,8},{2,10},{4,12},{6,14},{8,0},{10,2},{12,4},{14,6},{1,9},{3,11}... | collective-permute-start | bytes 196616 | tf_op jit(solution)/shard_map/ppermute | solution.py:18
  24.3 7.0 %collective-permute-start.17 = (bf16[128,256]{1,0:T(8,128)(2,1)S(1)}, bf16[128,256]{1,0:T(8,128)(2,1)S(1)}, u32[]{:S(2)}, u32[]{:S(2)}) collective-permute-start(bf16[128,256]{1,0:T(8,128)(2,1)S(1)} %fusion.45), channel_id=1, source_target_pairs={{0,8},{2,10},{4,12},{6,14},{8,0},{10,2},{12,4},{14,6},{1,9},{3,11}... | collective-permute-start | bytes 196616 | tf_op jit(solution)/shard_map/ppermute | solution.py:18
  27.8 4.9 %collective-permute-start.3 = (bf16[128,256]{1,0:T(8,128)(2,1)S(1)}, bf16[128,256]{1,0:T(8,128)(2,1)S(1)}, u32[]{:S(2)}, u32[]{:S(2)}) collective-permute-start(bf16[128,256]{1,0:T(8,128)(2,1)S(1)} %multiply_convert_fusion.3), channel_id=1, source_target_pairs={{0,4},{2,6},{4,0},{6,2},{8,12},{10,14},{12,8},{14,10},{1,5},{3,7},... | collective-permute-start | bytes 196616 | tf_op jit(solution)/shard_map/ppermute | solution.py:18
  29.9 4.8 %collective-permute-start.8 = (bf16[128,256]{1,0:T(8,128)(2,1)S(1)}, bf16[128,256]{1,0:T(8,128)(2,1)S(1)}, u32[]{:S(2)}, u32[]{:S(2)}) collective-permute-start(bf16[128,256]{1,0:T(8,128)(2,1)S(1)} %multiply_convert_fusion.2), channel_id=1, source_target_pairs={{0,2},{2,0},{4,6},{6,4},{8,10},{10,8},{12,14},{14,12},{1,3},{3,1},... | collective-permute-start | bytes 196616 | tf_op jit(solution)/shard_map/ppermute | solution.py:18
  30.6 4.9 %collective-permute-start.13 = (bf16[128,256]{1,0:T(8,128)(2,1)S(1)}, bf16[128,256]{1,0:T(8,128)(2,1)S(1)}, u32[]{:S(2)}, u32[]{:S(2)}) collective-permute-start(bf16[128,256]{1,0:T(8,128)(2,1)S(1)} %multiply_convert_fusion.1), channel_id=1, source_target_pairs={{0,4},{2,6},{4,0},{6,2},{8,12},{10,14},{12,8},{14,10},{1,5},{3,7},... | collective-permute-start | bytes 196616 | tf_op jit(solution)/shard_map/ppermute | solution.py:18
  31.4 5.8 %collective-permute-start.18 = (bf16[128,256]{1,0:T(8,128)(2,1)S(1)}, bf16[128,256]{1,0:T(8,128)(2,1)S(1)}, u32[]{:S(2)}, u32[]{:S(2)}) collective-permute-start(bf16[128,256]{1,0:T(8,128)(2,1)S(1)} %multiply_convert_fusion), channel_id=1, source_target_pairs={{0,2},{2,0},{4,6},{6,4},{8,10},{10,8},{12,14},{14,12},{1,3},{3,1},... | collective-permute-start | bytes 196616 | tf_op jit(solution)/shard_map/ppermute | solution.py:18
  32.7 10.0 %collective-permute-start.4 = (bf16[128,512]{1,0:T(8,128)(2,1)S(1)}, bf16[128,512]{1,0:T(8,128)(2,1)S(1)}, u32[]{:S(2)}, u32[]{:S(2)}) collective-permute-start(bf16[128,512]{1,0:T(8,128)(2,1)S(1)} %pad_maximum_fusion.1), channel_id=1, source_target_pairs={{0,2},{2,0},{4,6},{6,4},{8,10},{10,8},{12,14},{14,12},{1,3},{3,1},... | collective-permute-start | bytes 393224 | tf_op jit(solution)/shard_map/ppermute | solution.py:18
  34.8 5.0 %collective-permute-start.9 = (bf16[128,512]{1,0:T(8,128)(2,1)S(1)}, bf16[128,512]{1,0:T(8,128)(2,1)S(1)}, u32[]{:S(2)}, u32[]{:S(2)}) collective-permute-start(bf16[128,512]{1,0:T(8,128)(2,1)S(1)} %pad_maximum_fusion.2), channel_id=1, source_target_pairs={{0,4},{2,6},{4,0},{6,2},{8,12},{10,14},{12,8},{14,10},{1,5},{3,7},... | collective-permute-start | bytes 393224 | tf_op jit(solution)/shard_map/ppermute | solution.py:18
  35.5 5.0 %collective-permute-start.14 = (bf16[128,512]{1,0:T(8,128)(2,1)S(1)}, bf16[128,512]{1,0:T(8,128)(2,1)S(1)}, u32[]{:S(2)}, u32[]{:S(2)}) collective-permute-start(bf16[128,512]{1,0:T(8,128)(2,1)S(1)} %pad_maximum_fusion.3), channel_id=1, source_target_pairs={{0,2},{2,0},{4,6},{6,4},{8,10},{10,8},{12,14},{14,12},{1,3},{3,1},... | collective-permute-start | bytes 393224 | tf_op jit(solution)/shard_map/ppermute | solution.py:18
  37.2 5.0 %collective-permute-start.19 = (bf16[128,512]{1,0:T(8,128)(2,1)S(1)}, bf16[128,512]{1,0:T(8,128)(2,1)S(1)}, u32[]{:S(2)}, u32[]{:S(2)}) collective-permute-start(bf16[128,512]{1,0:T(8,128)(2,1)S(1)} %pad_maximum_fusion.4), channel_id=1, source_target_pairs={{0,4},{2,6},{4,0},{6,2},{8,12},{10,14},{12,8},{14,10},{1,5},{3,7},... | collective-permute-start | bytes 393224 | tf_op jit(solution)/shard_map/ppermute | solution.py:18
  43.2 1.6 %collective-permute-start.20 = (f32[512,128]{1,0:T(8,128)S(1)}, f32[512,128]{1,0:T(8,128)S(1)}, u32[]{:S(2)}, u32[]{:S(2)}) collective-permute-start(f32[512,128]{1,0:T(8,128)S(1)} %fusion.2.mine_ref), channel_id=1, source_target_pairs={{0,1},{1,0},{2,3},{3,2},{4,5},{5,4},{6,7},{7,6},{8,9},{9,8},{10,11... | collective-permute-start | bytes 786440 | tf_op jit(solution)/shard_map/ppermute | solution.py:18
  45.3 5.1 %collective-permute-start.21 = (f32[72,128]{1,0:T(8,128)S(1)}, f32[72,128]{1,0:T(8,128)S(1)}, u32[]{:S(2)}, u32[]{:S(2)}) collective-permute-start(f32[72,128]{1,0:T(8,128)S(1)} %get-tuple-element.17), channel_id=1, source_target_pairs={{1,5},{3,7},{5,1},{7,3},{9,13},{11,15},{13,9},{15,11},{17,21},{19,... | collective-permute-start | bytes 110600 | tf_op jit(solution)/shard_map/ppermute | solution.py:36
  46.0 4.5 %collective-permute-start.22 = (f32[72,128]{1,0:T(8,128)S(1)}, f32[72,128]{1,0:T(8,128)S(1)}, u32[]{:S(2)}, u32[]{:S(2)}) collective-permute-start(f32[72,128]{1,0:T(8,128)S(1)} %get-tuple-element.17), channel_id=1, source_target_pairs={{0,2},{1,7},{2,0},{3,5},{4,6},{5,3},{6,4},{7,1},{8,10},{9,15},{10,... | collective-permute-start | bytes 110600 | tf_op jit(solution)/shard_map/ppermute | solution.py:36
  46.6 4.9 %collective-permute-start.23 = (f32[72,128]{1,0:T(8,128)S(1)}, f32[72,128]{1,0:T(8,128)S(1)}, u32[]{:S(2)}, u32[]{:S(2)}) collective-permute-start(f32[72,128]{1,0:T(8,128)S(1)} %get-tuple-element.17), channel_id=1, source_target_pairs={{0,8},{1,13},{2,10},{3,15},{4,12},{5,9},{6,14},{7,11},{8,0},{9,5},... | collective-permute-start | bytes 110600 | tf_op jit(solution)/shard_map/ppermute | solution.py:36
  48.3 6.8 %collective-permute-start.24 = (f32[72,128]{1,0:T(8,128)S(1)}, f32[72,128]{1,0:T(8,128)S(1)}, u32[]{:S(2)}, u32[]{:S(2)}) collective-permute-start(f32[72,128]{1,0:T(8,128)S(1)} %get-tuple-element.17), channel_id=1, source_target_pairs={{0,10},{1,15},{2,8},{3,13},{4,14},{5,11},{6,12},{7,9},{8,2},{9,7},... | collective-permute-start | bytes 110600 | tf_op jit(solution)/shard_map/ppermute | solution.py:36
  55.1 2.0 %collective-permute-start.25 = (f32[72,128]{1,0:T(8,128)S(1)}, f32[72,128]{1,0:T(8,128)S(1)}, u32[]{:S(2)}, u32[]{:S(2)}) collective-permute-start(f32[72,128]{1,0:T(8,128)S(1)} %add_add_fusion), channel_id=1, source_target_pairs={{0,1},{1,0},{2,3},{3,2},{4,5},{5,4},{6,7},{7,6},{8,9},{9,8},{10,11... | collective-permute-start | bytes 110600 | tf_op jit(solution)/shard_map/ppermute | solution.py:18
  61.3 6.4 %collective-permute-start.26 = (bf16[2,2,16,1024]{3,2,1,0:T(8,128)(2,1)S(1)}, bf16[2,2,16,1024]{3,2,1,0:T(8,128)(2,1)S(1)}, u32[]{:S(2)}, u32[]{:S(2)}) collective-permute-start(bf16[2,2,16,1024]{3,2,1,0:T(8,128)(2,1)S(1)} %fusion.22), channel_id=1, source_target_pairs={{0,2},{2,0},{4,6},{6,4},{8,10},{10,8},{12,14},{14,12},{1,3},{3,1},... | collective-permute-start | bytes 393224 | tf_op jit(solution)/shard_map/ppermute | solution.py:18
  62.4 6.4 %collective-permute-start.29 = (bf16[2,2,16,1024]{3,2,0,1:T(8,128)(2,1)S(1)}, bf16[2,2,16,1024]{3,2,0,1:T(8,128)(2,1)S(1)}, u32[]{:S(2)}, u32[]{:S(2)}) collective-permute-start(bf16[2,2,16,1024]{3,2,0,1:T(8,128)(2,1)S(1)} %fusion.23), channel_id=1, source_target_pairs={{0,4},{2,6},{4,0},{6,2},{8,12},{10,14},{12,8},{14,10},{1,5},{3,7},... | collective-permute-start | bytes 393224 | tf_op jit(solution)/shard_map/ppermute | solution.py:18
  62.6 7.5 %collective-permute-start.32 = (bf16[2,2,16,1024]{3,2,1,0:T(8,128)(2,1)S(1)}, bf16[2,2,16,1024]{3,2,1,0:T(8,128)(2,1)S(1)}, u32[]{:S(2)}, u32[]{:S(2)}) collective-permute-start(bf16[2,2,16,1024]{3,2,1,0:T(8,128)(2,1)S(1)} %fusion.24), channel_id=1, source_target_pairs={{0,2},{2,0},{4,6},{6,4},{8,10},{10,8},{12,14},{14,12},{1,3},{3,1},... | collective-permute-start | bytes 393224 | tf_op jit(solution)/shard_map/ppermute | solution.py:18
  63.7 8.2 %collective-permute-start.35 = (bf16[2,2,16,1024]{3,2,0,1:T(8,128)(2,1)S(1)}, bf16[2,2,16,1024]{3,2,0,1:T(8,128)(2,1)S(1)}, u32[]{:S(2)}, u32[]{:S(2)}) collective-permute-start(bf16[2,2,16,1024]{3,2,0,1:T(8,128)(2,1)S(1)} %fusion.25), channel_id=1, source_target_pairs={{0,4},{2,6},{4,0},{6,2},{8,12},{10,14},{12,8},{14,10},{1,5},{3,7},... | collective-permute-start | bytes 393224 | tf_op jit(solution)/shard_map/ppermute | solution.py:18
  67.7 5.5 %collective-permute-start.27 = (bf16[2,16,1024]{2,1,0:T(8,128)(2,1)S(1)}, bf16[2,16,1024]{2,1,0:T(8,128)(2,1)S(1)}, u32[]{:S(2)}, u32[]{:S(2)}) collective-permute-start(bf16[2,16,1024]{2,1,0:T(8,128)(2,1)S(1)} %fusion.30), channel_id=1, source_target_pairs={{0,4},{2,6},{4,0},{6,2},{8,12},{10,14},{12,8},{14,10},{1,5},{3,7},... | collective-permute-start | bytes 196616 | tf_op jit(solution)/shard_map/ppermute | solution.py:18
  68.9 6.1 %collective-permute-start.30 = (bf16[2,16,1024]{2,1,0:T(8,128)(2,1)S(1)}, bf16[2,16,1024]{2,1,0:T(8,128)(2,1)S(1)}, u32[]{:S(2)}, u32[]{:S(2)}) collective-permute-start(bf16[2,16,1024]{2,1,0:T(8,128)(2,1)S(1)} %fusion.31), channel_id=1, source_target_pairs={{0,2},{2,0},{4,6},{6,4},{8,10},{10,8},{12,14},{14,12},{1,3},{3,1},... | collective-permute-start | bytes 196616 | tf_op jit(solution)/shard_map/ppermute | solution.py:18
  70.1 9.2 %collective-permute-start.33 = (bf16[2,16,1024]{2,1,0:T(8,128)(2,1)S(1)}, bf16[2,16,1024]{2,1,0:T(8,128)(2,1)S(1)}, u32[]{:S(2)}, u32[]{:S(2)}) collective-permute-start(bf16[2,16,1024]{2,1,0:T(8,128)(2,1)S(1)} %fusion.32), channel_id=1, source_target_pairs={{0,8},{2,10},{4,12},{6,14},{8,0},{10,2},{12,4},{14,6},{1,9},{3,11}... | collective-permute-start | bytes 196616 | tf_op jit(solution)/shard_map/ppermute | solution.py:18
  72.0 8.5 %collective-permute-start.36 = (bf16[2,16,1024]{2,1,0:T(8,128)(2,1)S(1)}, bf16[2,16,1024]{2,1,0:T(8,128)(2,1)S(1)}, u32[]{:S(2)}, u32[]{:S(2)}) collective-permute-start(bf16[2,16,1024]{2,1,0:T(8,128)(2,1)S(1)} %fusion.33), channel_id=1, source_target_pairs={{0,8},{2,10},{4,12},{6,14},{8,0},{10,2},{12,4},{14,6},{1,9},{3,11}... | collective-permute-start | bytes 196616 | tf_op jit(solution)/shard_map/ppermute | solution.py:18
  73.3 7.9 %collective-permute-start.28 = (bf16[16,1024]{1,0:T(8,128)(2,1)S(1)}, bf16[16,1024]{1,0:T(8,128)(2,1)S(1)}, u32[]{:S(2)}, u32[]{:S(2)}) collective-permute-start(bf16[16,1024]{1,0:T(8,128)(2,1)S(1)} %fusion.38), channel_id=1, source_target_pairs={{0,8},{2,10},{4,12},{6,14},{8,0},{10,2},{12,4},{14,6},{1,9},{3,11}... | collective-permute-start | bytes 98312 | tf_op jit(solution)/shard_map/ppermute | solution.py:18
  75.1 6.1 %collective-permute-start.31 = (bf16[16,1024]{1,0:T(8,128)(2,1)S(1)}, bf16[16,1024]{1,0:T(8,128)(2,1)S(1)}, u32[]{:S(2)}, u32[]{:S(2)}) collective-permute-start(bf16[16,1024]{1,0:T(8,128)(2,1)S(1)} %fusion.39), channel_id=1, source_target_pairs={{0,8},{2,10},{4,12},{6,14},{8,0},{10,2},{12,4},{14,6},{1,9},{3,11}... | collective-permute-start | bytes 98312 | tf_op jit(solution)/shard_map/ppermute | solution.py:18
  79.3 4.0 %collective-permute-start.34 = (bf16[16,1024]{1,0:T(8,128)(2,1)S(1)}, bf16[16,1024]{1,0:T(8,128)(2,1)S(1)}, u32[]{:S(2)}, u32[]{:S(2)}) collective-permute-start(bf16[16,1024]{1,0:T(8,128)(2,1)S(1)} %fusion.40), channel_id=1, source_target_pairs={{0,4},{2,6},{4,0},{6,2},{8,12},{10,14},{12,8},{14,10},{1,5},{3,7},... | collective-permute-start | bytes 98312 | tf_op jit(solution)/shard_map/ppermute | solution.py:18
  80.5 4.0 %collective-permute-start.37 = (bf16[16,1024]{1,0:T(8,128)(2,1)S(1)}, bf16[16,1024]{1,0:T(8,128)(2,1)S(1)}, u32[]{:S(2)}, u32[]{:S(2)}) collective-permute-start(bf16[16,1024]{1,0:T(8,128)(2,1)S(1)} %fusion.41), channel_id=1, source_target_pairs={{0,2},{2,0},{4,6},{6,4},{8,10},{10,8},{12,14},{14,12},{1,3},{3,1},... | collective-permute-start | bytes 98312 | tf_op jit(solution)/shard_map/ppermute | solution.py:18

commit v31 on v25

--- a/solution.py
+++ b/solution.py
@@ -9,7 +9,7 @@
 from jax.sharding import PartitionSpec as P
 
 CHUNKS = 4
-TILE = 512
+TILE = 256
 KERNEL_VMEM = 50 * 2**20
 
 

time: 81.8 us -> 83.3 us (1.018)
  Pallas kernels: 8.67 us -> 10.2 us
    pallas_call x2, Pallas kernels: 4.07 us -> 5.56 us  [first_product(): pl.pallas_call(functools.partial(sketch_kernel, begin), out_shape=[jax.Sh...]
  transfers between devices with their start and end apart: 38 -> 38, of which waited for: 19 -> 19; matrix products, arithmetic and copies ran while one was open for 3% -> 3% of each run, Pallas kernels for 2% -> 3%
where the time goes in v31:
time: 83.3 us; the launch traced here: 83 us
  starting transfers between devices  44.6 us (54%)
  waiting for transfers between devices  22.3 us (27%)
  Pallas kernels  10.2 us (12%)
  other arithmetic  2.12 us (3%)
  matrix products  1.77 us (2%)
  between operations  1.11 us (1%)
  local copies, waits for them, and re-layouts  1.05 us (1%)
    ppermute x34, starting transfers between devices, swap(): return lax.ppermute(value, axis, [(i, i ^ distance) for i in range(size)])  39.5 us
    ppermute x34, waiting for transfers between devices, swap(): return lax.ppermute(value, axis, [(i, i ^ distance) for i in range(size)])  19.6 us
    pallas_call x2, Pallas kernels, first_product(): pl.pallas_call(functools.partial(sketch_kernel, begin), out_shape=[jax.Sh...  5.56 us
    ppermute x4, starting transfers between devices, row_sum(): terms.append(lax.ppermute(value, ('row', 'col'), pairs))  5.1 us
    pallas_call x1, Pallas kernels, make_basis(): pl.pallas_call(functools.partial(basis_kernel, root_rows), out_shape=[jax...  4.1 us
    ppermute x4, waiting for transfers between devices, row_sum(): terms.append(lax.ppermute(value, ('row', 'col'), pairs))  2.68 us
    dot_general x4, matrix products, per_device(): lax.dot_general(activations[:, span], shared, (((1,), (1,)), ((), ())), p...  1.77 us
  transfers between devices with their start and end apart: 38, of which 19 were waited for; matrix products, arithmetic and copies ran while one was open for 3% of the time, Pallas kernels for 3%

profile of v31, /device:TPU:0, one launch (start us, length us, event | category | flops | bytes accessed | tf_op | source)
XLA Modules:
  0.0 83.0 jit_solution(6881995118579112410)
XLA Ops:
  0.7 0.9 %copy-done = bf16[512,128]{1,0:T(8,128)(2,1)S(1)} copy-done((bf16[512,128]{1,0:T(8,128)(2,1)S(1)}, bf16[512,128]{1,0:T(8,128)(2,1)}, u32[]{:S(2)}) %copy-start) | copy-done | bytes 131096
  1.6 2.8 %first_product.3 = (f32[128,1024]{1,0:T(8,128)S(1)}, f32[128,1024]{1,0:T(8,128)S(1)}) custom-call(bf16[512,128]{1,0:T(8,128)(2,1)S(1)} %copy-done, bf16[512,4096]{1,0:T(8,128)(2,1)} %slab_ref.5), custom_call_target="tpu_custom_call" | custom-call | flops 268435456 | bytes 2097152 | tf_op jit(solution)/shard_map/first_product/pallas_call | solution.py:117
  4.4 3.1 %collective-permute-start.15 = (bf16[128,512]{1,0:T(8,128)(2,1)S(1)}, bf16[128,512]{1,0:T(8,128)(2,1)S(1)}, u32[]{:S(2)}, u32[]{:S(2)}) collective-permute-start(bf16[128,512]{1,0:T(8,128)(2,1)S(1)} %select_convert_fusion.4), channel_id=1, source_target_pairs={{0,4},{2,6},{4,0},{6,2},{8,12},{10,14},{12,8},{14,10},{1,5},{3,7},... | collective-permute-start | bytes 393224 | tf_op jit(solution)/shard_map/ppermute | solution.py:18
  7.5 1.6 %collective-permute-start.10 = (bf16[128,512]{1,0:T(8,128)(2,1)S(1)}, bf16[128,512]{1,0:T(8,128)(2,1)S(1)}, u32[]{:S(2)}, u32[]{:S(2)}) collective-permute-start(bf16[128,512]{1,0:T(8,128)(2,1)S(1)} %select_convert_fusion.5), channel_id=1, source_target_pairs={{0,2},{2,0},{4,6},{6,4},{8,10},{10,8},{12,14},{14,12},{1,3},{3,1},... | collective-permute-start | bytes 393224 | tf_op jit(solution)/shard_map/ppermute | solution.py:18
  9.1 2.8 %first_product.2 = (f32[128,1024]{1,0:T(8,128)S(1)}, f32[128,1024]{1,0:T(8,128)S(1)}) custom-call(bf16[512,128]{1,0:T(8,128)(2,1)S(1)} %copy-done.1, bf16[512,4096]{1,0:T(8,128)(2,1)} %slab_ref.5), custom_call_target="tpu_custom_call" | custom-call | flops 268435456 | bytes 2097152 | tf_op jit(solution)/shard_map/first_product/pallas_call | solution.py:117
  12.7 2.0 %collective-permute-start.16 = (bf16[128,256]{1,0:T(8,128)(2,1)S(1)}, bf16[128,256]{1,0:T(8,128)(2,1)S(1)}, u32[]{:S(2)}, u32[]{:S(2)}) collective-permute-start(bf16[128,256]{1,0:T(8,128)(2,1)S(1)} %select_convert_fusion.12), channel_id=1, source_target_pairs={{0,2},{2,0},{4,6},{6,4},{8,10},{10,8},{12,14},{14,12},{1,3},{3,1},... | collective-permute-start | bytes 196616 | tf_op jit(solution)/shard_map/ppermute | solution.py:18
  14.7 1.6 %collective-permute-start.11 = (bf16[128,256]{1,0:T(8,128)(2,1)S(1)}, bf16[128,256]{1,0:T(8,128)(2,1)S(1)}, u32[]{:S(2)}, u32[]{:S(2)}) collective-permute-start(bf16[128,256]{1,0:T(8,128)(2,1)S(1)} %select_convert_fusion.13), channel_id=1, source_target_pairs={{0,4},{2,6},{4,0},{6,2},{8,12},{10,14},{12,8},{14,10},{1,5},{3,7},... | collective-permute-start | bytes 196616 | tf_op jit(solution)/shard_map/ppermute | solution.py:18
  16.4 1.2 %collective-permute-done.5 = bf16[128,512]{1,0:T(8,128)(2,1)S(1)} collective-permute-done((bf16[128,512]{1,0:T(8,128)(2,1)S(1)}, bf16[128,512]{1,0:T(8,128)(2,1)S(1)}, u32[]{:S(2)}, u32[]{:S(2)}) %collective-permute-start.5) | collective-permute-done | bytes 131104 | tf_op jit(solution)/shard_map/ppermute | solution.py:18
  17.7 0.6 collective-permute-start.6
  18.4 1.6 %collective-permute-start.1 = (bf16[128,256]{1,0:T(8,128)(2,1)S(1)}, bf16[128,256]{1,0:T(8,128)(2,1)S(1)}, u32[]{:S(2)}, u32[]{:S(2)}) collective-permute-start(bf16[128,256]{1,0:T(8,128)(2,1)S(1)} %select_convert_fusion.15), channel_id=1, source_target_pairs={{0,4},{2,6},{4,0},{6,2},{8,12},{10,14},{12,8},{14,10},{1,5},{3,7},... | collective-permute-start | bytes 196616 | tf_op jit(solution)/shard_map/ppermute | solution.py:18
  20.0 2.7 %collective-permute-start.17 = (bf16[128,256]{1,0:T(8,128)(2,1)S(1)}, bf16[128,256]{1,0:T(8,128)(2,1)S(1)}, u32[]{:S(2)}, u32[]{:S(2)}) collective-permute-start(bf16[128,256]{1,0:T(8,128)(2,1)S(1)} %fusion.41), channel_id=1, source_target_pairs={{0,8},{2,10},{4,12},{6,14},{8,0},{10,2},{12,4},{14,6},{1,9},{3,11}... | collective-permute-start | bytes 196616 | tf_op jit(solution)/shard_map/ppermute | solution.py:18
  23.2 2.7 %collective-permute-start.7 = (bf16[128,256]{1,0:T(8,128)(2,1)S(1)}, bf16[128,256]{1,0:T(8,128)(2,1)S(1)}, u32[]{:S(2)}, u32[]{:S(2)}) collective-permute-start(bf16[128,256]{1,0:T(8,128)(2,1)S(1)} %fusion.39), channel_id=1, source_target_pairs={{0,8},{2,10},{4,12},{6,14},{8,0},{10,2},{12,4},{14,6},{1,9},{3,11}... | collective-permute-start | bytes 196616 | tf_op jit(solution)/shard_map/ppermute | solution.py:18
  26.2 2.4 %collective-permute-done.17 = bf16[128,256]{1,0:T(8,128)(2,1)S(1)} collective-permute-done((bf16[128,256]{1,0:T(8,128)(2,1)S(1)}, bf16[128,256]{1,0:T(8,128)(2,1)S(1)}, u32[]{:S(2)}, u32[]{:S(2)}) %collective-permute-start.17) | collective-permute-done | bytes 65568 | tf_op jit(solution)/shard_map/ppermute | solution.py:18
  28.7 2.7 %collective-permute-done.12 = bf16[128,256]{1,0:T(8,128)(2,1)S(1)} collective-permute-done((bf16[128,256]{1,0:T(8,128)(2,1)S(1)}, bf16[128,256]{1,0:T(8,128)(2,1)S(1)}, u32[]{:S(2)}, u32[]{:S(2)}) %collective-permute-start.12) | collective-permute-done | bytes 65568 | tf_op jit(solution)/shard_map/ppermute | solution.py:18
  31.6 0.6 collective-permute-done.7
  32.2 0.6 collective-permute-start.8
  32.9 0.9 %collective-permute-start.3 = (bf16[128,256]{1,0:T(8,128)(2,1)S(1)}, bf16[128,256]{1,0:T(8,128)(2,1)S(1)}, u32[]{:S(2)}, u32[]{:S(2)}) collective-permute-start(bf16[128,256]{1,0:T(8,128)(2,1)S(1)} %multiply_convert_fusion.3), channel_id=1, source_target_pairs={{0,4},{2,6},{4,0},{6,2},{8,12},{10,14},{12,8},{14,10},{1,5},{3,7},... | collective-permute-start | bytes 196616 | tf_op jit(solution)/shard_map/ppermute | solution.py:18
  33.8 1.3 %collective-permute-start.19 = (bf16[128,512]{1,0:T(8,128)(2,1)S(1)}, bf16[128,512]{1,0:T(8,128)(2,1)S(1)}, u32[]{:S(2)}, u32[]{:S(2)}) collective-permute-start(bf16[128,512]{1,0:T(8,128)(2,1)S(1)} %pad_maximum_fusion.4), channel_id=1, source_target_pairs={{0,4},{2,6},{4,0},{6,2},{8,12},{10,14},{12,8},{14,10},{1,5},{3,7},... | collective-permute-start | bytes 393224 | tf_op jit(solution)/shard_map/ppermute | solution.py:18
  35.1 1.4 %collective-permute-done.13 = bf16[128,256]{1,0:T(8,128)(2,1)S(1)} collective-permute-done((bf16[128,256]{1,0:T(8,128)(2,1)S(1)}, bf16[128,256]{1,0:T(8,128)(2,1)S(1)}, u32[]{:S(2)}, u32[]{:S(2)}) %collective-permute-start.13) | collective-permute-done | bytes 65568 | tf_op jit(solution)/shard_map/ppermute | solution.py:18
  37.1 1.4 %collective-permute-start.9 = (bf16[128,512]{1,0:T(8,128)(2,1)S(1)}, bf16[128,512]{1,0:T(8,128)(2,1)S(1)}, u32[]{:S(2)}, u32[]{:S(2)}) collective-permute-start(bf16[128,512]{1,0:T(8,128)(2,1)S(1)} %pad_maximum_fusion.2), channel_id=1, source_target_pairs={{0,4},{2,6},{4,0},{6,2},{8,12},{10,14},{12,8},{14,10},{1,5},{3,7},... | collective-permute-start | bytes 393224 | tf_op jit(solution)/shard_map/ppermute | solution.py:18
  38.6 0.9 %collective-permute-start.4 = (bf16[128,512]{1,0:T(8,128)(2,1)S(1)}, bf16[128,512]{1,0:T(8,128)(2,1)S(1)}, u32[]{:S(2)}, u32[]{:S(2)}) collective-permute-start(bf16[128,512]{1,0:T(8,128)(2,1)S(1)} %pad_maximum_fusion.1), channel_id=1, source_target_pairs={{0,2},{2,0},{4,6},{6,4},{8,10},{10,8},{12,14},{14,12},{1,3},{3,1},... | collective-permute-start | bytes 393224 | tf_op jit(solution)/shard_map/ppermute | solution.py:18
  39.5 1.1 %collective-permute-done.19 = bf16[128,512]{1,0:T(8,128)(2,1)S(1)} collective-permute-done((bf16[128,512]{1,0:T(8,128)(2,1)S(1)}, bf16[128,512]{1,0:T(8,128)(2,1)S(1)}, u32[]{:S(2)}, u32[]{:S(2)}) %collective-permute-start.19) | collective-permute-done | bytes 131104 | tf_op jit(solution)/shard_map/ppermute | solution.py:18
  42.7 0.9 %collective-permute-done.4 = bf16[128,512]{1,0:T(8,128)(2,1)S(1)} collective-permute-done((bf16[128,512]{1,0:T(8,128)(2,1)S(1)}, bf16[128,512]{1,0:T(8,128)(2,1)S(1)}, u32[]{:S(2)}, u32[]{:S(2)}) %collective-permute-start.4) | collective-permute-done | bytes 131104 | tf_op jit(solution)/shard_map/ppermute | solution.py:18
  44.2 1.5 %collective-permute-done.20.other_ref = f32[512,128]{1,0:T(8,128)S(1)} collective-permute-done((f32[512,128]{1,0:T(8,128)S(1)}, f32[512,128]{1,0:T(8,128)S(1)}, u32[]{:S(2)}, u32[]{:S(2)}) %collective-permute-start.20) | collective-permute-done | bytes 262176 | tf_op jit(solution)/shard_map/ppermute | solution.py:18
  46.2 2.3 %collective-permute-start.24 = (f32[72,128]{1,0:T(8,128)S(1)}, f32[72,128]{1,0:T(8,128)S(1)}, u32[]{:S(2)}, u32[]{:S(2)}) collective-permute-start(f32[72,128]{1,0:T(8,128)S(1)} %get-tuple-element.17), channel_id=1, source_target_pairs={{0,10},{1,15},{2,8},{3,13},{4,14},{5,11},{6,12},{7,9},{8,2},{9,7},... | collective-permute-start | bytes 110600 | tf_op jit(solution)/shard_map/ppermute | solution.py:36
  48.5 1.0 %collective-permute-start.23 = (f32[72,128]{1,0:T(8,128)S(1)}, f32[72,128]{1,0:T(8,128)S(1)}, u32[]{:S(2)}, u32[]{:S(2)}) collective-permute-start(f32[72,128]{1,0:T(8,128)S(1)} %get-tuple-element.17), channel_id=1, source_target_pairs={{0,8},{1,13},{2,10},{3,15},{4,12},{5,9},{6,14},{7,11},{8,0},{9,5},... | collective-permute-start | bytes 110600 | tf_op jit(solution)/shard_map/ppermute | solution.py:36
  49.5 1.2 %collective-permute-start.22 = (f32[72,128]{1,0:T(8,128)S(1)}, f32[72,128]{1,0:T(8,128)S(1)}, u32[]{:S(2)}, u32[]{:S(2)}) collective-permute-start(f32[72,128]{1,0:T(8,128)S(1)} %get-tuple-element.17), channel_id=1, source_target_pairs={{0,2},{1,7},{2,0},{3,5},{4,6},{5,3},{6,4},{7,1},{8,10},{9,15},{10,... | collective-permute-start | bytes 110600 | tf_op jit(solution)/shard_map/ppermute | solution.py:36
  50.7 0.7 collective-permute-start.21
  51.3 1.5 %collective-permute-done.24 = f32[72,128]{1,0:T(8,128)S(1)} collective-permute-done((f32[72,128]{1,0:T(8,128)S(1)}, f32[72,128]{1,0:T(8,128)S(1)}, u32[]{:S(2)}, u32[]{:S(2)}) %collective-permute-start.24) | collective-permute-done | bytes 36896 | tf_op jit(solution)/shard_map/ppermute | solution.py:36
  52.8 1.2 %collective-permute-done.23 = f32[72,128]{1,0:T(8,128)S(1)} collective-permute-done((f32[72,128]{1,0:T(8,128)S(1)}, f32[72,128]{1,0:T(8,128)S(1)}, u32[]{:S(2)}, u32[]{:S(2)}) %collective-permute-start.23) | collective-permute-done | bytes 36896 | tf_op jit(solution)/shard_map/ppermute | solution.py:36
  54.0 1.3 %collective-permute-start.25 = (f32[72,128]{1,0:T(8,128)S(1)}, f32[72,128]{1,0:T(8,128)S(1)}, u32[]{:S(2)}, u32[]{:S(2)}) collective-permute-start(f32[72,128]{1,0:T(8,128)S(1)} %add_add_fusion), channel_id=1, source_target_pairs={{0,1},{1,0},{2,3},{3,2},{4,5},{5,4},{6,7},{7,6},{8,9},{9,8},{10,11... | collective-permute-start | bytes 110600 | tf_op jit(solution)/shard_map/ppermute | solution.py:18
  55.4 0.9 %collective-permute-done.25 = f32[72,128]{1,0:T(8,128)S(1)} collective-permute-done((f32[72,128]{1,0:T(8,128)S(1)}, f32[72,128]{1,0:T(8,128)S(1)}, u32[]{:S(2)}, u32[]{:S(2)}) %collective-permute-start.25) | collective-permute-done | bytes 36896 | tf_op jit(solution)/shard_map/ppermute | solution.py:18
  56.2 4.1 %make_basis.1 = (f32[512,128]{1,0:T(8,128)}, f32[128,1024]{1,0:T(8,128)S(1)}, f32[128,1024]{1,0:T(8,128)S(1)}, f32[128,1024]{1,0:T(8,128)S(1)}, f32[128,1024]{1,0:T(8,128)S(1)}) custom-call(f32[72,128]{1,0:T(8,128)S(1)} %add.116.gram_ref, f32[128,512]{1,0:T(8,128)S(1)} %get-tuple-element.18.sketch_ref, bf16[512,4096]{1,0:T(8,128)(2,1)} %slab_ref.5), custom_call_target="tpu_custom_call" | custom-call | tf_op jit(solution)/shard_map/make_basis/pallas_call | solution.py:279
  60.4 0.9 %collective-permute-start.26 = (bf16[2,2,16,1024]{3,2,0,1:T(8,128)(2,1)S(1)}, bf16[2,2,16,1024]{3,2,0,1:T(8,128)(2,1)S(1)}, u32[]{:S(2)}, u32[]{:S(2)}) collective-permute-start(bf16[2,2,16,1024]{3,2,0,1:T(8,128)(2,1)S(1)} %fusion.22), channel_id=1, source_target_pairs={{0,2},{2,0},{4,6},{6,4},{8,10},{10,8},{12,14},{14,12},{1,3},{3,1},... | collective-permute-start | bytes 393224 | tf_op jit(solution)/shard_map/ppermute | solution.py:18
  61.4 1.8 %collective-permute-start.29 = (bf16[2,2,16,1024]{3,2,0,1:T(8,128)(2,1)S(1)}, bf16[2,2,16,1024]{3,2,0,1:T(8,128)(2,1)S(1)}, u32[]{:S(2)}, u32[]{:S(2)}) collective-permute-start(bf16[2,2,16,1024]{3,2,0,1:T(8,128)(2,1)S(1)} %fusion.23), channel_id=1, source_target_pairs={{0,4},{2,6},{4,0},{6,2},{8,12},{10,14},{12,8},{14,10},{1,5},{3,7},... | collective-permute-start | bytes 393224 | tf_op jit(solution)/shard_map/ppermute | solution.py:18
  63.3 1.3 %collective-permute-start.32 = (bf16[2,2,16,1024]{3,2,0,1:T(8,128)(2,1)S(1)}, bf16[2,2,16,1024]{3,2,0,1:T(8,128)(2,1)S(1)}, u32[]{:S(2)}, u32[]{:S(2)}) collective-permute-start(bf16[2,2,16,1024]{3,2,0,1:T(8,128)(2,1)S(1)} %fusion.24), channel_id=1, source_target_pairs={{0,2},{2,0},{4,6},{6,4},{8,10},{10,8},{12,14},{14,12},{1,3},{3,1},... | collective-permute-start | bytes 393224 | tf_op jit(solution)/shard_map/ppermute | solution.py:18
  65.0 1.7 %collective-permute-done.26 = bf16[2,2,16,1024]{3,2,0,1:T(8,128)(2,1)S(1)} collective-permute-done((bf16[2,2,16,1024]{3,2,0,1:T(8,128)(2,1)S(1)}, bf16[2,2,16,1024]{3,2,0,1:T(8,128)(2,1)S(1)}, u32[]{:S(2)}, u32[]{:S(2)}) %collective-permute-start.26) | collective-permute-done | bytes 131104 | tf_op jit(solution)/shard_map/ppermute | solution.py:18
  66.8 1.9 %collective-permute-start.27 = (bf16[2,16,1024]{2,1,0:T(8,128)(2,1)S(1)}, bf16[2,16,1024]{2,1,0:T(8,128)(2,1)S(1)}, u32[]{:S(2)}, u32[]{:S(2)}) collective-permute-start(bf16[2,16,1024]{2,1,0:T(8,128)(2,1)S(1)} %fusion.26), channel_id=1, source_target_pairs={{0,4},{2,6},{4,0},{6,2},{8,12},{10,14},{12,8},{14,10},{1,5},{3,7},... | collective-permute-start | bytes 196616 | tf_op jit(solution)/shard_map/ppermute | solution.py:18
  68.7 0.9 %collective-permute-start.30 = (bf16[2,16,1024]{2,1,0:T(8,128)(2,1)S(1)}, bf16[2,16,1024]{2,1,0:T(8,128)(2,1)S(1)}, u32[]{:S(2)}, u32[]{:S(2)}) collective-permute-start(bf16[2,16,1024]{2,1,0:T(8,128)(2,1)S(1)} %fusion.27), channel_id=1, source_target_pairs={{0,2},{2,0},{4,6},{6,4},{8,10},{10,8},{12,14},{14,12},{1,3},{3,1},... | collective-permute-start | bytes 196616 | tf_op jit(solution)/shard_map/ppermute | solution.py:18
  69.7 1.3 %collective-permute-start.33 = (bf16[2,16,1024]{2,1,0:T(8,128)(2,1)S(1)}, bf16[2,16,1024]{2,1,0:T(8,128)(2,1)S(1)}, u32[]{:S(2)}, u32[]{:S(2)}) collective-permute-start(bf16[2,16,1024]{2,1,0:T(8,128)(2,1)S(1)} %fusion.28), channel_id=1, source_target_pairs={{0,4},{2,6},{4,0},{6,2},{8,12},{10,14},{12,8},{14,10},{1,5},{3,7},... | collective-permute-start | bytes 196616 | tf_op jit(solution)/shard_map/ppermute | solution.py:18
  71.1 0.9 %collective-permute-start.36 = (bf16[2,16,1024]{2,1,0:T(8,128)(2,1)S(1)}, bf16[2,16,1024]{2,1,0:T(8,128)(2,1)S(1)}, u32[]{:S(2)}, u32[]{:S(2)}) collective-permute-start(bf16[2,16,1024]{2,1,0:T(8,128)(2,1)S(1)} %fusion.29), channel_id=1, source_target_pairs={{0,2},{2,0},{4,6},{6,4},{8,10},{10,8},{12,14},{14,12},{1,3},{3,1},... | collective-permute-start | bytes 196616 | tf_op jit(solution)/shard_map/ppermute | solution.py:18
  72.0 1.8 %collective-permute-start.28 = (bf16[16,1024]{1,0:T(8,128)(2,1)S(1)}, bf16[16,1024]{1,0:T(8,128)(2,1)S(1)}, u32[]{:S(2)}, u32[]{:S(2)}) collective-permute-start(bf16[16,1024]{1,0:T(8,128)(2,1)S(1)} %fusion.34), channel_id=1, source_target_pairs={{0,8},{2,10},{4,12},{6,14},{8,0},{10,2},{12,4},{14,6},{1,9},{3,11}... | collective-permute-start | bytes 98312 | tf_op jit(solution)/shard_map/ppermute | solution.py:18
  73.9 1.2 %collective-permute-start.31 = (bf16[16,1024]{1,0:T(8,128)(2,1)S(1)}, bf16[16,1024]{1,0:T(8,128)(2,1)S(1)}, u32[]{:S(2)}, u32[]{:S(2)}) collective-permute-start(bf16[16,1024]{1,0:T(8,128)(2,1)S(1)} %fusion.35), channel_id=1, source_target_pairs={{0,8},{2,10},{4,12},{6,14},{8,0},{10,2},{12,4},{14,6},{1,9},{3,11}... | collective-permute-start | bytes 98312 | tf_op jit(solution)/shard_map/ppermute | solution.py:18
  75.2 1.8 %collective-permute-start.34 = (bf16[16,1024]{1,0:T(8,128)(2,1)S(1)}, bf16[16,1024]{1,0:T(8,128)(2,1)S(1)}, u32[]{:S(2)}, u32[]{:S(2)}) collective-permute-start(bf16[16,1024]{1,0:T(8,128)(2,1)S(1)} %fusion.36), channel_id=1, source_target_pairs={{0,8},{2,10},{4,12},{6,14},{8,0},{10,2},{12,4},{14,6},{1,9},{3,11}... | collective-permute-start | bytes 98312 | tf_op jit(solution)/shard_map/ppermute | solution.py:18
  77.1 1.2 %collective-permute-start.37 = (bf16[16,1024]{1,0:T(8,128)(2,1)S(1)}, bf16[16,1024]{1,0:T(8,128)(2,1)S(1)}, u32[]{:S(2)}, u32[]{:S(2)}) collective-permute-start(bf16[16,1024]{1,0:T(8,128)(2,1)S(1)} %fusion.37), channel_id=1, source_target_pairs={{0,8},{2,10},{4,12},{6,14},{8,0},{10,2},{12,4},{14,6},{1,9},{3,11}... | collective-permute-start | bytes 98312 | tf_op jit(solution)/shard_map/ppermute | solution.py:18
  78.3 1.3 %collective-permute-done.31 = bf16[16,1024]{1,0:T(8,128)(2,1)S(1)} collective-permute-done((bf16[16,1024]{1,0:T(8,128)(2,1)S(1)}, bf16[16,1024]{1,0:T(8,128)(2,1)S(1)}, u32[]{:S(2)}, u32[]{:S(2)}) %collective-permute-start.31) | collective-permute-done | bytes 32800 | tf_op jit(solution)/shard_map/ppermute | solution.py:18
  80.2 2.1 %collective-permute-done.37 = bf16[16,1024]{1,0:T(8,128)(2,1)S(1)} collective-permute-done((bf16[16,1024]{1,0:T(8,128)(2,1)S(1)}, bf16[16,1024]{1,0:T(8,128)(2,1)S(1)}, u32[]{:S(2)}, u32[]{:S(2)}) %collective-permute-start.37) | collective-permute-done | bytes 32800 | tf_op jit(solution)/shard_map/ppermute | solution.py:18
  82.3 0.7 pad_maximum_fusion
  (105 shorter events, 7.7 us)
Async XLA Ops:
  0.6 0.9 %copy-start = (bf16[512,128]{1,0:T(8,128)(2,1)S(1)}, bf16[512,128]{1,0:T(8,128)(2,1)}, u32[]{:S(2)}) copy-start(bf16[512,128]{1,0:T(8,128)(2,1)} %start_ref.3) | copy-start | bytes 393220
  1.6 7.5 %copy-start.1 = (bf16[512,128]{1,0:T(8,128)(2,1)S(1)}, bf16[512,128]{1,0:T(8,128)(2,1)}, u32[]{:S(2)}) copy-start(bf16[512,128]{1,0:T(8,128)(2,1)} %start_ref.3) | copy-start | bytes 393220
  4.4 8.2 %collective-permute-start.15 = (bf16[128,512]{1,0:T(8,128)(2,1)S(1)}, bf16[128,512]{1,0:T(8,128)(2,1)S(1)}, u32[]{:S(2)}, u32[]{:S(2)}) collective-permute-start(bf16[128,512]{1,0:T(8,128)(2,1)S(1)} %select_convert_fusion.4), channel_id=1, source_target_pairs={{0,4},{2,6},{4,0},{6,2},{8,12},{10,14},{12,8},{14,10},{1,5},{3,7},... | collective-permute-start | bytes 393224 | tf_op jit(solution)/shard_map/ppermute | solution.py:18
  7.5 7.1 %collective-permute-start.10 = (bf16[128,512]{1,0:T(8,128)(2,1)S(1)}, bf16[128,512]{1,0:T(8,128)(2,1)S(1)}, u32[]{:S(2)}, u32[]{:S(2)}) collective-permute-start(bf16[128,512]{1,0:T(8,128)(2,1)S(1)} %select_convert_fusion.5), channel_id=1, source_target_pairs={{0,2},{2,0},{4,6},{6,4},{8,10},{10,8},{12,14},{14,12},{1,3},{3,1},... | collective-permute-start | bytes 393224 | tf_op jit(solution)/shard_map/ppermute | solution.py:18
  11.9 5.7 %collective-permute-start.5 = (bf16[128,512]{1,0:T(8,128)(2,1)S(1)}, bf16[128,512]{1,0:T(8,128)(2,1)S(1)}, u32[]{:S(2)}, u32[]{:S(2)}) collective-permute-start(bf16[128,512]{1,0:T(8,128)(2,1)S(1)} %select_convert_fusion.6), channel_id=1, source_target_pairs={{0,4},{2,6},{4,0},{6,2},{8,12},{10,14},{12,8},{14,10},{1,5},{3,7},... | collective-permute-start | bytes 393224 | tf_op jit(solution)/shard_map/ppermute | solution.py:18
  12.4 5.9 %collective-permute-start = (bf16[128,512]{1,0:T(8,128)(2,1)S(1)}, bf16[128,512]{1,0:T(8,128)(2,1)S(1)}, u32[]{:S(2)}, u32[]{:S(2)}) collective-permute-start(bf16[128,512]{1,0:T(8,128)(2,1)S(1)} %select_convert_fusion.7), channel_id=1, source_target_pairs={{0,2},{2,0},{4,6},{6,4},{8,10},{10,8},{12,14},{14,12},{1,3},{3,1},... | collective-permute-start | bytes 393224 | tf_op jit(solution)/shard_map/ppermute | solution.py:18
  12.7 7.3 %collective-permute-start.16 = (bf16[128,256]{1,0:T(8,128)(2,1)S(1)}, bf16[128,256]{1,0:T(8,128)(2,1)S(1)}, u32[]{:S(2)}, u32[]{:S(2)}) collective-permute-start(bf16[128,256]{1,0:T(8,128)(2,1)S(1)} %select_convert_fusion.12), channel_id=1, source_target_pairs={{0,2},{2,0},{4,6},{6,4},{8,10},{10,8},{12,14},{14,12},{1,3},{3,1},... | collective-permute-start | bytes 196616 | tf_op jit(solution)/shard_map/ppermute | solution.py:18
  14.7 25.9 %copy-start.2 = (bf16[512,4096]{1,0:T(8,128)(2,1)S(1)}, bf16[512,4096]{1,0:T(8,128)(2,1)}, u32[]{:S(2)}) copy-start(bf16[512,4096]{1,0:T(8,128)(2,1)} %slab_ref.5) | copy-start | bytes 12582916
  14.7 8.0 %collective-permute-start.11 = (bf16[128,256]{1,0:T(8,128)(2,1)S(1)}, bf16[128,256]{1,0:T(8,128)(2,1)S(1)}, u32[]{:S(2)}, u32[]{:S(2)}) collective-permute-start(bf16[128,256]{1,0:T(8,128)(2,1)S(1)} %select_convert_fusion.13), channel_id=1, source_target_pairs={{0,4},{2,6},{4,0},{6,2},{8,12},{10,14},{12,8},{14,10},{1,5},{3,7},... | collective-permute-start | bytes 196616 | tf_op jit(solution)/shard_map/ppermute | solution.py:18
  17.7 5.4 %collective-permute-start.6 = (bf16[128,256]{1,0:T(8,128)(2,1)S(1)}, bf16[128,256]{1,0:T(8,128)(2,1)S(1)}, u32[]{:S(2)}, u32[]{:S(2)}) collective-permute-start(bf16[128,256]{1,0:T(8,128)(2,1)S(1)} %select_convert_fusion.14), channel_id=1, source_target_pairs={{0,2},{2,0},{4,6},{6,4},{8,10},{10,8},{12,14},{14,12},{1,3},{3,1},... | collective-permute-start | bytes 196616 | tf_op jit(solution)/shard_map/ppermute | solution.py:18
  18.4 7.4 %collective-permute-start.1 = (bf16[128,256]{1,0:T(8,128)(2,1)S(1)}, bf16[128,256]{1,0:T(8,128)(2,1)S(1)}, u32[]{:S(2)}, u32[]{:S(2)}) collective-permute-start(bf16[128,256]{1,0:T(8,128)(2,1)S(1)} %select_convert_fusion.15), channel_id=1, source_target_pairs={{0,4},{2,6},{4,0},{6,2},{8,12},{10,14},{12,8},{14,10},{1,5},{3,7},... | collective-permute-start | bytes 196616 | tf_op jit(solution)/shard_map/ppermute | solution.py:18
  20.0 8.6 %collective-permute-start.17 = (bf16[128,256]{1,0:T(8,128)(2,1)S(1)}, bf16[128,256]{1,0:T(8,128)(2,1)S(1)}, u32[]{:S(2)}, u32[]{:S(2)}) collective-permute-start(bf16[128,256]{1,0:T(8,128)(2,1)S(1)} %fusion.41), channel_id=1, source_target_pairs={{0,8},{2,10},{4,12},{6,14},{8,0},{10,2},{12,4},{14,6},{1,9},{3,11}... | collective-permute-start | bytes 196616 | tf_op jit(solution)/shard_map/ppermute | solution.py:18
  22.7 8.7 %collective-permute-start.12 = (bf16[128,256]{1,0:T(8,128)(2,1)S(1)}, bf16[128,256]{1,0:T(8,128)(2,1)S(1)}, u32[]{:S(2)}, u32[]{:S(2)}) collective-permute-start(bf16[128,256]{1,0:T(8,128)(2,1)S(1)} %fusion.40), channel_id=1, source_target_pairs={{0,8},{2,10},{4,12},{6,14},{8,0},{10,2},{12,4},{14,6},{1,9},{3,11}... | collective-permute-start | bytes 196616 | tf_op jit(solution)/shard_map/ppermute | solution.py:18
  23.2 9.0 %collective-permute-start.7 = (bf16[128,256]{1,0:T(8,128)(2,1)S(1)}, bf16[128,256]{1,0:T(8,128)(2,1)S(1)}, u32[]{:S(2)}, u32[]{:S(2)}) collective-permute-start(bf16[128,256]{1,0:T(8,128)(2,1)S(1)} %fusion.39), channel_id=1, source_target_pairs={{0,8},{2,10},{4,12},{6,14},{8,0},{10,2},{12,4},{14,6},{1,9},{3,11}... | collective-permute-start | bytes 196616 | tf_op jit(solution)/shard_map/ppermute | solution.py:18
  25.8 7.0 %collective-permute-start.2 = (bf16[128,256]{1,0:T(8,128)(2,1)S(1)}, bf16[128,256]{1,0:T(8,128)(2,1)S(1)}, u32[]{:S(2)}, u32[]{:S(2)}) collective-permute-start(bf16[128,256]{1,0:T(8,128)(2,1)S(1)} %fusion.38), channel_id=1, source_target_pairs={{0,8},{2,10},{4,12},{6,14},{8,0},{10,2},{12,4},{14,6},{1,9},{3,11}... | collective-permute-start | bytes 196616 | tf_op jit(solution)/shard_map/ppermute | solution.py:18
  28.6 5.2 %collective-permute-start.18 = (bf16[128,256]{1,0:T(8,128)(2,1)S(1)}, bf16[128,256]{1,0:T(8,128)(2,1)S(1)}, u32[]{:S(2)}, u32[]{:S(2)}) collective-permute-start(bf16[128,256]{1,0:T(8,128)(2,1)S(1)} %multiply_convert_fusion), channel_id=1, source_target_pairs={{0,2},{2,0},{4,6},{6,4},{8,10},{10,8},{12,14},{14,12},{1,3},{3,1},... | collective-permute-start | bytes 196616 | tf_op jit(solution)/shard_map/ppermute | solution.py:18
  31.5 5.0 %collective-permute-start.13 = (bf16[128,256]{1,0:T(8,128)(2,1)S(1)}, bf16[128,256]{1,0:T(8,128)(2,1)S(1)}, u32[]{:S(2)}, u32[]{:S(2)}) collective-permute-start(bf16[128,256]{1,0:T(8,128)(2,1)S(1)} %multiply_convert_fusion.1), channel_id=1, source_target_pairs={{0,4},{2,6},{4,0},{6,2},{8,12},{10,14},{12,8},{14,10},{1,5},{3,7},... | collective-permute-start | bytes 196616 | tf_op jit(solution)/shard_map/ppermute | solution.py:18
  32.2 4.9 %collective-permute-start.8 = (bf16[128,256]{1,0:T(8,128)(2,1)S(1)}, bf16[128,256]{1,0:T(8,128)(2,1)S(1)}, u32[]{:S(2)}, u32[]{:S(2)}) collective-permute-start(bf16[128,256]{1,0:T(8,128)(2,1)S(1)} %multiply_convert_fusion.2), channel_id=1, source_target_pairs={{0,2},{2,0},{4,6},{6,4},{8,10},{10,8},{12,14},{14,12},{1,3},{3,1},... | collective-permute-start | bytes 196616 | tf_op jit(solution)/shard_map/ppermute | solution.py:18
  32.9 5.6 %collective-permute-start.3 = (bf16[128,256]{1,0:T(8,128)(2,1)S(1)}, bf16[128,256]{1,0:T(8,128)(2,1)S(1)}, u32[]{:S(2)}, u32[]{:S(2)}) collective-permute-start(bf16[128,256]{1,0:T(8,128)(2,1)S(1)} %multiply_convert_fusion.3), channel_id=1, source_target_pairs={{0,4},{2,6},{4,0},{6,2},{8,12},{10,14},{12,8},{14,10},{1,5},{3,7},... | collective-permute-start | bytes 196616 | tf_op jit(solution)/shard_map/ppermute | solution.py:18
  33.8 6.8 %collective-permute-start.19 = (bf16[128,512]{1,0:T(8,128)(2,1)S(1)}, bf16[128,512]{1,0:T(8,128)(2,1)S(1)}, u32[]{:S(2)}, u32[]{:S(2)}) collective-permute-start(bf16[128,512]{1,0:T(8,128)(2,1)S(1)} %pad_maximum_fusion.4), channel_id=1, source_target_pairs={{0,4},{2,6},{4,0},{6,2},{8,12},{10,14},{12,8},{14,10},{1,5},{3,7},... | collective-permute-start | bytes 393224 | tf_op jit(solution)/shard_map/ppermute | solution.py:18
  36.5 5.0 %collective-permute-start.14 = (bf16[128,512]{1,0:T(8,128)(2,1)S(1)}, bf16[128,512]{1,0:T(8,128)(2,1)S(1)}, u32[]{:S(2)}, u32[]{:S(2)}) collective-permute-start(bf16[128,512]{1,0:T(8,128)(2,1)S(1)} %pad_maximum_fusion.3), channel_id=1, source_target_pairs={{0,2},{2,0},{4,6},{6,4},{8,10},{10,8},{12,14},{14,12},{1,3},{3,1},... | collective-permute-start | bytes 393224 | tf_op jit(solution)/shard_map/ppermute | solution.py:18
  37.1 5.0 %collective-permute-start.9 = (bf16[128,512]{1,0:T(8,128)(2,1)S(1)}, bf16[128,512]{1,0:T(8,128)(2,1)S(1)}, u32[]{:S(2)}, u32[]{:S(2)}) collective-permute-start(bf16[128,512]{1,0:T(8,128)(2,1)S(1)} %pad_maximum_fusion.2), channel_id=1, source_target_pairs={{0,4},{2,6},{4,0},{6,2},{8,12},{10,14},{12,8},{14,10},{1,5},{3,7},... | collective-permute-start | bytes 393224 | tf_op jit(solution)/shard_map/ppermute | solution.py:18
  38.6 5.0 %collective-permute-start.4 = (bf16[128,512]{1,0:T(8,128)(2,1)S(1)}, bf16[128,512]{1,0:T(8,128)(2,1)S(1)}, u32[]{:S(2)}, u32[]{:S(2)}) collective-permute-start(bf16[128,512]{1,0:T(8,128)(2,1)S(1)} %pad_maximum_fusion.1), channel_id=1, source_target_pairs={{0,2},{2,0},{4,6},{6,4},{8,10},{10,8},{12,14},{14,12},{1,3},{3,1},... | collective-permute-start | bytes 393224 | tf_op jit(solution)/shard_map/ppermute | solution.py:18
  44.1 1.6 %collective-permute-start.20 = (f32[512,128]{1,0:T(8,128)S(1)}, f32[512,128]{1,0:T(8,128)S(1)}, u32[]{:S(2)}, u32[]{:S(2)}) collective-permute-start(f32[512,128]{1,0:T(8,128)S(1)} %fusion.2.mine_ref), channel_id=1, source_target_pairs={{0,1},{1,0},{2,3},{3,2},{4,5},{5,4},{6,7},{7,6},{8,9},{9,8},{10,11... | collective-permute-start | bytes 786440 | tf_op jit(solution)/shard_map/ppermute | solution.py:18
  46.2 6.6 %collective-permute-start.24 = (f32[72,128]{1,0:T(8,128)S(1)}, f32[72,128]{1,0:T(8,128)S(1)}, u32[]{:S(2)}, u32[]{:S(2)}) collective-permute-start(f32[72,128]{1,0:T(8,128)S(1)} %get-tuple-element.17), channel_id=1, source_target_pairs={{0,10},{1,15},{2,8},{3,13},{4,14},{5,11},{6,12},{7,9},{8,2},{9,7},... | collective-permute-start | bytes 110600 | tf_op jit(solution)/shard_map/ppermute | solution.py:36
  48.5 5.5 %collective-permute-start.23 = (f32[72,128]{1,0:T(8,128)S(1)}, f32[72,128]{1,0:T(8,128)S(1)}, u32[]{:S(2)}, u32[]{:S(2)}) collective-permute-start(f32[72,128]{1,0:T(8,128)S(1)} %get-tuple-element.17), channel_id=1, source_target_pairs={{0,8},{1,13},{2,10},{3,15},{4,12},{5,9},{6,14},{7,11},{8,0},{9,5},... | collective-permute-start | bytes 110600 | tf_op jit(solution)/shard_map/ppermute | solution.py:36
  49.5 4.5 %collective-permute-start.22 = (f32[72,128]{1,0:T(8,128)S(1)}, f32[72,128]{1,0:T(8,128)S(1)}, u32[]{:S(2)}, u32[]{:S(2)}) collective-permute-start(f32[72,128]{1,0:T(8,128)S(1)} %get-tuple-element.17), channel_id=1, source_target_pairs={{0,2},{1,7},{2,0},{3,5},{4,6},{5,3},{6,4},{7,1},{8,10},{9,15},{10,... | collective-permute-start | bytes 110600 | tf_op jit(solution)/shard_map/ppermute | solution.py:36
  50.7 3.3 %collective-permute-start.21 = (f32[72,128]{1,0:T(8,128)S(1)}, f32[72,128]{1,0:T(8,128)S(1)}, u32[]{:S(2)}, u32[]{:S(2)}) collective-permute-start(f32[72,128]{1,0:T(8,128)S(1)} %get-tuple-element.17), channel_id=1, source_target_pairs={{1,5},{3,7},{5,1},{7,3},{9,13},{11,15},{13,9},{15,11},{17,21},{19,... | collective-permute-start | bytes 110600 | tf_op jit(solution)/shard_map/ppermute | solution.py:36
  54.0 2.2 %collective-permute-start.25 = (f32[72,128]{1,0:T(8,128)S(1)}, f32[72,128]{1,0:T(8,128)S(1)}, u32[]{:S(2)}, u32[]{:S(2)}) collective-permute-start(f32[72,128]{1,0:T(8,128)S(1)} %add_add_fusion), channel_id=1, source_target_pairs={{0,1},{1,0},{2,3},{3,2},{4,5},{5,4},{6,7},{7,6},{8,9},{9,8},{10,11... | collective-permute-start | bytes 110600 | tf_op jit(solution)/shard_map/ppermute | solution.py:18
  60.4 6.3 %collective-permute-start.26 = (bf16[2,2,16,1024]{3,2,0,1:T(8,128)(2,1)S(1)}, bf16[2,2,16,1024]{3,2,0,1:T(8,128)(2,1)S(1)}, u32[]{:S(2)}, u32[]{:S(2)}) collective-permute-start(bf16[2,2,16,1024]{3,2,0,1:T(8,128)(2,1)S(1)} %fusion.22), channel_id=1, source_target_pairs={{0,2},{2,0},{4,6},{6,4},{8,10},{10,8},{12,14},{14,12},{1,3},{3,1},... | collective-permute-start | bytes 393224 | tf_op jit(solution)/shard_map/ppermute | solution.py:18
  61.4 7.3 %collective-permute-start.29 = (bf16[2,2,16,1024]{3,2,0,1:T(8,128)(2,1)S(1)}, bf16[2,2,16,1024]{3,2,0,1:T(8,128)(2,1)S(1)}, u32[]{:S(2)}, u32[]{:S(2)}) collective-permute-start(bf16[2,2,16,1024]{3,2,0,1:T(8,128)(2,1)S(1)} %fusion.23), channel_id=1, source_target_pairs={{0,4},{2,6},{4,0},{6,2},{8,12},{10,14},{12,8},{14,10},{1,5},{3,7},... | collective-permute-start | bytes 393224 | tf_op jit(solution)/shard_map/ppermute | solution.py:18
  63.3 6.4 %collective-permute-start.32 = (bf16[2,2,16,1024]{3,2,0,1:T(8,128)(2,1)S(1)}, bf16[2,2,16,1024]{3,2,0,1:T(8,128)(2,1)S(1)}, u32[]{:S(2)}, u32[]{:S(2)}) collective-permute-start(bf16[2,2,16,1024]{3,2,0,1:T(8,128)(2,1)S(1)} %fusion.24), channel_id=1, source_target_pairs={{0,2},{2,0},{4,6},{6,4},{8,10},{10,8},{12,14},{14,12},{1,3},{3,1},... | collective-permute-start | bytes 393224 | tf_op jit(solution)/shard_map/ppermute | solution.py:18
  64.6 6.4 %collective-permute-start.35 = (bf16[2,2,16,1024]{3,2,0,1:T(8,128)(2,1)S(1)}, bf16[2,2,16,1024]{3,2,0,1:T(8,128)(2,1)S(1)}, u32[]{:S(2)}, u32[]{:S(2)}) collective-permute-start(bf16[2,2,16,1024]{3,2,0,1:T(8,128)(2,1)S(1)} %fusion.25), channel_id=1, source_target_pairs={{0,4},{2,6},{4,0},{6,2},{8,12},{10,14},{12,8},{14,10},{1,5},{3,7},... | collective-permute-start | bytes 393224 | tf_op jit(solution)/shard_map/ppermute | solution.py:18
  66.8 5.2 %collective-permute-start.27 = (bf16[2,16,1024]{2,1,0:T(8,128)(2,1)S(1)}, bf16[2,16,1024]{2,1,0:T(8,128)(2,1)S(1)}, u32[]{:S(2)}, u32[]{:S(2)}) collective-permute-start(bf16[2,16,1024]{2,1,0:T(8,128)(2,1)S(1)} %fusion.26), channel_id=1, source_target_pairs={{0,4},{2,6},{4,0},{6,2},{8,12},{10,14},{12,8},{14,10},{1,5},{3,7},... | collective-permute-start | bytes 196616 | tf_op jit(solution)/shard_map/ppermute | solution.py:18
  68.7 5.1 %collective-permute-start.30 = (bf16[2,16,1024]{2,1,0:T(8,128)(2,1)S(1)}, bf16[2,16,1024]{2,1,0:T(8,128)(2,1)S(1)}, u32[]{:S(2)}, u32[]{:S(2)}) collective-permute-start(bf16[2,16,1024]{2,1,0:T(8,128)(2,1)S(1)} %fusion.27), channel_id=1, source_target_pairs={{0,2},{2,0},{4,6},{6,4},{8,10},{10,8},{12,14},{14,12},{1,3},{3,1},... | collective-permute-start | bytes 196616 | tf_op jit(solution)/shard_map/ppermute | solution.py:18
  69.7 5.4 %collective-permute-start.33 = (bf16[2,16,1024]{2,1,0:T(8,128)(2,1)S(1)}, bf16[2,16,1024]{2,1,0:T(8,128)(2,1)S(1)}, u32[]{:S(2)}, u32[]{:S(2)}) collective-permute-start(bf16[2,16,1024]{2,1,0:T(8,128)(2,1)S(1)} %fusion.28), channel_id=1, source_target_pairs={{0,4},{2,6},{4,0},{6,2},{8,12},{10,14},{12,8},{14,10},{1,5},{3,7},... | collective-permute-start | bytes 196616 | tf_op jit(solution)/shard_map/ppermute | solution.py:18
  71.1 5.9 %collective-permute-start.36 = (bf16[2,16,1024]{2,1,0:T(8,128)(2,1)S(1)}, bf16[2,16,1024]{2,1,0:T(8,128)(2,1)S(1)}, u32[]{:S(2)}, u32[]{:S(2)}) collective-permute-start(bf16[2,16,1024]{2,1,0:T(8,128)(2,1)S(1)} %fusion.29), channel_id=1, source_target_pairs={{0,2},{2,0},{4,6},{6,4},{8,10},{10,8},{12,14},{14,12},{1,3},{3,1},... | collective-permute-start | bytes 196616 | tf_op jit(solution)/shard_map/ppermute | solution.py:18
  72.0 6.3 %collective-permute-start.28 = (bf16[16,1024]{1,0:T(8,128)(2,1)S(1)}, bf16[16,1024]{1,0:T(8,128)(2,1)S(1)}, u32[]{:S(2)}, u32[]{:S(2)}) collective-permute-start(bf16[16,1024]{1,0:T(8,128)(2,1)S(1)} %fusion.34), channel_id=1, source_target_pairs={{0,8},{2,10},{4,12},{6,14},{8,0},{10,2},{12,4},{14,6},{1,9},{3,11}... | collective-permute-start | bytes 98312 | tf_op jit(solution)/shard_map/ppermute | solution.py:18
  73.9 5.7 %collective-permute-start.31 = (bf16[16,1024]{1,0:T(8,128)(2,1)S(1)}, bf16[16,1024]{1,0:T(8,128)(2,1)S(1)}, u32[]{:S(2)}, u32[]{:S(2)}) collective-permute-start(bf16[16,1024]{1,0:T(8,128)(2,1)S(1)} %fusion.35), channel_id=1, source_target_pairs={{0,8},{2,10},{4,12},{6,14},{8,0},{10,2},{12,4},{14,6},{1,9},{3,11}... | collective-permute-start | bytes 98312 | tf_op jit(solution)/shard_map/ppermute | solution.py:18
  75.2 5.0 %collective-permute-start.34 = (bf16[16,1024]{1,0:T(8,128)(2,1)S(1)}, bf16[16,1024]{1,0:T(8,128)(2,1)S(1)}, u32[]{:S(2)}, u32[]{:S(2)}) collective-permute-start(bf16[16,1024]{1,0:T(8,128)(2,1)S(1)} %fusion.36), channel_id=1, source_target_pairs={{0,8},{2,10},{4,12},{6,14},{8,0},{10,2},{12,4},{14,6},{1,9},{3,11}... | collective-permute-start | bytes 98312 | tf_op jit(solution)/shard_map/ppermute | solution.py:18
  77.1 5.2 %collective-permute-start.37 = (bf16[16,1024]{1,0:T(8,128)(2,1)S(1)}, bf16[16,1024]{1,0:T(8,128)(2,1)S(1)}, u32[]{:S(2)}, u32[]{:S(2)}) collective-permute-start(bf16[16,1024]{1,0:T(8,128)(2,1)S(1)} %fusion.37), channel_id=1, source_target_pairs={{0,8},{2,10},{4,12},{6,14},{8,0},{10,2},{12,4},{14,6},{1,9},{3,11}... | collective-permute-start | bytes 98312 | tf_op jit(solution)/shard_map/ppermute | solution.py:18

commit v32 on v31

--- a/solution.py
+++ b/solution.py
@@ -9,7 +9,7 @@
 from jax.sharding import PartitionSpec as P
 
 CHUNKS = 4
-TILE = 256
+TILE = 1024
 KERNEL_VMEM = 50 * 2**20
 
 

time: 83.3 us -> 81.5 us (0.978)
  Pallas kernels: 10.2 us -> 8.4 us
    pallas_call x2, Pallas kernels: 5.56 us -> 3.8 us  [first_product(): pl.pallas_call(functools.partial(sketch_kernel, begin), out_shape=[jax.Sh...]
  transfers between devices with their start and end apart: 38 -> 38, of which waited for: 19 -> 19; matrix products, arithmetic and copies ran while one was open for 3% -> 3% of each run, Pallas kernels for 3% -> 2%
where the time goes in v32:
time: 81.5 us; the launch traced here: 81.3 us
  starting transfers between devices  44.5 us (55%)
  waiting for transfers between devices  22.3 us (27%)
  Pallas kernels  8.4 us (10%)
  other arithmetic  2.12 us (3%)
  matrix products  1.77 us (2%)
  between operations  1.12 us (1%)
  local copies, waits for them, and re-layouts  1.05 us (1%)
    ppermute x34, starting transfers between devices, swap(): return lax.ppermute(value, axis, [(i, i ^ distance) for i in range(size)])  39.4 us
    ppermute x34, waiting for transfers between devices, swap(): return lax.ppermute(value, axis, [(i, i ^ distance) for i in range(size)])  19.6 us
    ppermute x4, starting transfers between devices, row_sum(): terms.append(lax.ppermute(value, ('row', 'col'), pairs))  5.1 us
    pallas_call x1, Pallas kernels, make_basis(): pl.pallas_call(functools.partial(basis_kernel, root_rows), out_shape=[jax...  4.1 us
    pallas_call x2, Pallas kernels, first_product(): pl.pallas_call(functools.partial(sketch_kernel, begin), out_shape=[jax.Sh...  3.8 us
    ppermute x4, waiting for transfers between devices, row_sum(): terms.append(lax.ppermute(value, ('row', 'col'), pairs))  2.67 us
    dot_general x4, matrix products, per_device(): lax.dot_general(activations[:, span], shared, (((1,), (1,)), ((), ())), p...  1.77 us
  transfers between devices with their start and end apart: 38, of which 19 were waited for; matrix products, arithmetic and copies ran while one was open for 3% of the time, Pallas kernels for 2%

profile of v32, /device:TPU:0, one launch (start us, length us, event | category | flops | bytes accessed | tf_op | source)
XLA Modules:
  0.0 81.3 jit_solution(18302810753059110123)
XLA Ops:
  0.7 0.9 %copy-done = bf16[512,128]{1,0:T(8,128)(2,1)S(1)} copy-done((bf16[512,128]{1,0:T(8,128)(2,1)S(1)}, bf16[512,128]{1,0:T(8,128)(2,1)}, u32[]{:S(2)}) %copy-start) | copy-done | bytes 131096
  1.6 1.9 %first_product.3 = (f32[128,1024]{1,0:T(8,128)S(1)}, f32[128,1024]{1,0:T(8,128)S(1)}) custom-call(bf16[512,128]{1,0:T(8,128)(2,1)S(1)} %copy-done, bf16[512,4096]{1,0:T(8,128)(2,1)} %slab_ref.5), custom_call_target="tpu_custom_call" | custom-call | flops 268435456 | bytes 2097152 | tf_op jit(solution)/shard_map/first_product/pallas_call | solution.py:117
  3.5 3.1 %collective-permute-start.15 = (bf16[128,512]{1,0:T(8,128)(2,1)S(1)}, bf16[128,512]{1,0:T(8,128)(2,1)S(1)}, u32[]{:S(2)}, u32[]{:S(2)}) collective-permute-start(bf16[128,512]{1,0:T(8,128)(2,1)S(1)} %select_convert_fusion.4), channel_id=1, source_target_pairs={{0,4},{2,6},{4,0},{6,2},{8,12},{10,14},{12,8},{14,10},{1,5},{3,7},... | collective-permute-start | bytes 393224 | tf_op jit(solution)/shard_map/ppermute | solution.py:18
  6.6 1.6 %collective-permute-start.10 = (bf16[128,512]{1,0:T(8,128)(2,1)S(1)}, bf16[128,512]{1,0:T(8,128)(2,1)S(1)}, u32[]{:S(2)}, u32[]{:S(2)}) collective-permute-start(bf16[128,512]{1,0:T(8,128)(2,1)S(1)} %select_convert_fusion.5), channel_id=1, source_target_pairs={{0,2},{2,0},{4,6},{6,4},{8,10},{10,8},{12,14},{14,12},{1,3},{3,1},... | collective-permute-start | bytes 393224 | tf_op jit(solution)/shard_map/ppermute | solution.py:18
  8.2 1.9 %first_product.2 = (f32[128,1024]{1,0:T(8,128)S(1)}, f32[128,1024]{1,0:T(8,128)S(1)}) custom-call(bf16[512,128]{1,0:T(8,128)(2,1)S(1)} %copy-done.1, bf16[512,4096]{1,0:T(8,128)(2,1)} %slab_ref.5), custom_call_target="tpu_custom_call" | custom-call | flops 268435456 | bytes 2097152 | tf_op jit(solution)/shard_map/first_product/pallas_call | solution.py:117
  10.9 2.0 %collective-permute-start.16 = (bf16[128,256]{1,0:T(8,128)(2,1)S(1)}, bf16[128,256]{1,0:T(8,128)(2,1)S(1)}, u32[]{:S(2)}, u32[]{:S(2)}) collective-permute-start(bf16[128,256]{1,0:T(8,128)(2,1)S(1)} %select_convert_fusion.12), channel_id=1, source_target_pairs={{0,2},{2,0},{4,6},{6,4},{8,10},{10,8},{12,14},{14,12},{1,3},{3,1},... | collective-permute-start | bytes 196616 | tf_op jit(solution)/shard_map/ppermute | solution.py:18
  13.0 1.7 %collective-permute-start.11 = (bf16[128,256]{1,0:T(8,128)(2,1)S(1)}, bf16[128,256]{1,0:T(8,128)(2,1)S(1)}, u32[]{:S(2)}, u32[]{:S(2)}) collective-permute-start(bf16[128,256]{1,0:T(8,128)(2,1)S(1)} %select_convert_fusion.13), channel_id=1, source_target_pairs={{0,4},{2,6},{4,0},{6,2},{8,12},{10,14},{12,8},{14,10},{1,5},{3,7},... | collective-permute-start | bytes 196616 | tf_op jit(solution)/shard_map/ppermute | solution.py:18
  14.6 1.2 %collective-permute-done.5 = bf16[128,512]{1,0:T(8,128)(2,1)S(1)} collective-permute-done((bf16[128,512]{1,0:T(8,128)(2,1)S(1)}, bf16[128,512]{1,0:T(8,128)(2,1)S(1)}, u32[]{:S(2)}, u32[]{:S(2)}) %collective-permute-start.5) | collective-permute-done | bytes 131104 | tf_op jit(solution)/shard_map/ppermute | solution.py:18
  15.9 0.6 collective-permute-start.6
  16.6 1.6 %collective-permute-start.1 = (bf16[128,256]{1,0:T(8,128)(2,1)S(1)}, bf16[128,256]{1,0:T(8,128)(2,1)S(1)}, u32[]{:S(2)}, u32[]{:S(2)}) collective-permute-start(bf16[128,256]{1,0:T(8,128)(2,1)S(1)} %select_convert_fusion.15), channel_id=1, source_target_pairs={{0,4},{2,6},{4,0},{6,2},{8,12},{10,14},{12,8},{14,10},{1,5},{3,7},... | collective-permute-start | bytes 196616 | tf_op jit(solution)/shard_map/ppermute | solution.py:18
  18.3 2.7 %collective-permute-start.17 = (bf16[128,256]{1,0:T(8,128)(2,1)S(1)}, bf16[128,256]{1,0:T(8,128)(2,1)S(1)}, u32[]{:S(2)}, u32[]{:S(2)}) collective-permute-start(bf16[128,256]{1,0:T(8,128)(2,1)S(1)} %fusion.41), channel_id=1, source_target_pairs={{0,8},{2,10},{4,12},{6,14},{8,0},{10,2},{12,4},{14,6},{1,9},{3,11}... | collective-permute-start | bytes 196616 | tf_op jit(solution)/shard_map/ppermute | solution.py:18
  21.4 2.7 %collective-permute-start.7 = (bf16[128,256]{1,0:T(8,128)(2,1)S(1)}, bf16[128,256]{1,0:T(8,128)(2,1)S(1)}, u32[]{:S(2)}, u32[]{:S(2)}) collective-permute-start(bf16[128,256]{1,0:T(8,128)(2,1)S(1)} %fusion.39), channel_id=1, source_target_pairs={{0,8},{2,10},{4,12},{6,14},{8,0},{10,2},{12,4},{14,6},{1,9},{3,11}... | collective-permute-start | bytes 196616 | tf_op jit(solution)/shard_map/ppermute | solution.py:18
  24.5 2.4 %collective-permute-done.17 = bf16[128,256]{1,0:T(8,128)(2,1)S(1)} collective-permute-done((bf16[128,256]{1,0:T(8,128)(2,1)S(1)}, bf16[128,256]{1,0:T(8,128)(2,1)S(1)}, u32[]{:S(2)}, u32[]{:S(2)}) %collective-permute-start.17) | collective-permute-done | bytes 65568 | tf_op jit(solution)/shard_map/ppermute | solution.py:18
  27.0 2.7 %collective-permute-done.12 = bf16[128,256]{1,0:T(8,128)(2,1)S(1)} collective-permute-done((bf16[128,256]{1,0:T(8,128)(2,1)S(1)}, bf16[128,256]{1,0:T(8,128)(2,1)S(1)}, u32[]{:S(2)}, u32[]{:S(2)}) %collective-permute-start.12) | collective-permute-done | bytes 65568 | tf_op jit(solution)/shard_map/ppermute | solution.py:18
  29.8 0.6 collective-permute-done.7
  30.4 0.6 collective-permute-start.8
  31.1 0.9 %collective-permute-start.3 = (bf16[128,256]{1,0:T(8,128)(2,1)S(1)}, bf16[128,256]{1,0:T(8,128)(2,1)S(1)}, u32[]{:S(2)}, u32[]{:S(2)}) collective-permute-start(bf16[128,256]{1,0:T(8,128)(2,1)S(1)} %multiply_convert_fusion.3), channel_id=1, source_target_pairs={{0,4},{2,6},{4,0},{6,2},{8,12},{10,14},{12,8},{14,10},{1,5},{3,7},... | collective-permute-start | bytes 196616 | tf_op jit(solution)/shard_map/ppermute | solution.py:18
  32.1 1.2 %collective-permute-start.19 = (bf16[128,512]{1,0:T(8,128)(2,1)S(1)}, bf16[128,512]{1,0:T(8,128)(2,1)S(1)}, u32[]{:S(2)}, u32[]{:S(2)}) collective-permute-start(bf16[128,512]{1,0:T(8,128)(2,1)S(1)} %pad_maximum_fusion.4), channel_id=1, source_target_pairs={{0,4},{2,6},{4,0},{6,2},{8,12},{10,14},{12,8},{14,10},{1,5},{3,7},... | collective-permute-start | bytes 393224 | tf_op jit(solution)/shard_map/ppermute | solution.py:18
  33.3 1.4 %collective-permute-done.13 = bf16[128,256]{1,0:T(8,128)(2,1)S(1)} collective-permute-done((bf16[128,256]{1,0:T(8,128)(2,1)S(1)}, bf16[128,256]{1,0:T(8,128)(2,1)S(1)}, u32[]{:S(2)}, u32[]{:S(2)}) %collective-permute-start.13) | collective-permute-done | bytes 65568 | tf_op jit(solution)/shard_map/ppermute | solution.py:18
  35.4 1.4 %collective-permute-start.9 = (bf16[128,512]{1,0:T(8,128)(2,1)S(1)}, bf16[128,512]{1,0:T(8,128)(2,1)S(1)}, u32[]{:S(2)}, u32[]{:S(2)}) collective-permute-start(bf16[128,512]{1,0:T(8,128)(2,1)S(1)} %pad_maximum_fusion.2), channel_id=1, source_target_pairs={{0,4},{2,6},{4,0},{6,2},{8,12},{10,14},{12,8},{14,10},{1,5},{3,7},... | collective-permute-start | bytes 393224 | tf_op jit(solution)/shard_map/ppermute | solution.py:18
  36.8 0.9 %collective-permute-start.4 = (bf16[128,512]{1,0:T(8,128)(2,1)S(1)}, bf16[128,512]{1,0:T(8,128)(2,1)S(1)}, u32[]{:S(2)}, u32[]{:S(2)}) collective-permute-start(bf16[128,512]{1,0:T(8,128)(2,1)S(1)} %pad_maximum_fusion.1), channel_id=1, source_target_pairs={{0,2},{2,0},{4,6},{6,4},{8,10},{10,8},{12,14},{14,12},{1,3},{3,1},... | collective-permute-start | bytes 393224 | tf_op jit(solution)/shard_map/ppermute | solution.py:18
  37.7 1.1 %collective-permute-done.19 = bf16[128,512]{1,0:T(8,128)(2,1)S(1)} collective-permute-done((bf16[128,512]{1,0:T(8,128)(2,1)S(1)}, bf16[128,512]{1,0:T(8,128)(2,1)S(1)}, u32[]{:S(2)}, u32[]{:S(2)}) %collective-permute-start.19) | collective-permute-done | bytes 131104 | tf_op jit(solution)/shard_map/ppermute | solution.py:18
  40.9 1.0 %collective-permute-done.4 = bf16[128,512]{1,0:T(8,128)(2,1)S(1)} collective-permute-done((bf16[128,512]{1,0:T(8,128)(2,1)S(1)}, bf16[128,512]{1,0:T(8,128)(2,1)S(1)}, u32[]{:S(2)}, u32[]{:S(2)}) %collective-permute-start.4) | collective-permute-done | bytes 131104 | tf_op jit(solution)/shard_map/ppermute | solution.py:18
  42.4 1.5 %collective-permute-done.20.other_ref = f32[512,128]{1,0:T(8,128)S(1)} collective-permute-done((f32[512,128]{1,0:T(8,128)S(1)}, f32[512,128]{1,0:T(8,128)S(1)}, u32[]{:S(2)}, u32[]{:S(2)}) %collective-permute-start.20) | collective-permute-done | bytes 262176 | tf_op jit(solution)/shard_map/ppermute | solution.py:18
  44.5 2.3 %collective-permute-start.24 = (f32[72,128]{1,0:T(8,128)S(1)}, f32[72,128]{1,0:T(8,128)S(1)}, u32[]{:S(2)}, u32[]{:S(2)}) collective-permute-start(f32[72,128]{1,0:T(8,128)S(1)} %get-tuple-element.17), channel_id=1, source_target_pairs={{0,10},{1,15},{2,8},{3,13},{4,14},{5,11},{6,12},{7,9},{8,2},{9,7},... | collective-permute-start | bytes 110600 | tf_op jit(solution)/shard_map/ppermute | solution.py:36
  46.7 1.0 %collective-permute-start.23 = (f32[72,128]{1,0:T(8,128)S(1)}, f32[72,128]{1,0:T(8,128)S(1)}, u32[]{:S(2)}, u32[]{:S(2)}) collective-permute-start(f32[72,128]{1,0:T(8,128)S(1)} %get-tuple-element.17), channel_id=1, source_target_pairs={{0,8},{1,13},{2,10},{3,15},{4,12},{5,9},{6,14},{7,11},{8,0},{9,5},... | collective-permute-start | bytes 110600 | tf_op jit(solution)/shard_map/ppermute | solution.py:36
  47.7 1.2 %collective-permute-start.22 = (f32[72,128]{1,0:T(8,128)S(1)}, f32[72,128]{1,0:T(8,128)S(1)}, u32[]{:S(2)}, u32[]{:S(2)}) collective-permute-start(f32[72,128]{1,0:T(8,128)S(1)} %get-tuple-element.17), channel_id=1, source_target_pairs={{0,2},{1,7},{2,0},{3,5},{4,6},{5,3},{6,4},{7,1},{8,10},{9,15},{10,... | collective-permute-start | bytes 110600 | tf_op jit(solution)/shard_map/ppermute | solution.py:36
  48.9 0.7 collective-permute-start.21
  49.6 1.5 %collective-permute-done.24 = f32[72,128]{1,0:T(8,128)S(1)} collective-permute-done((f32[72,128]{1,0:T(8,128)S(1)}, f32[72,128]{1,0:T(8,128)S(1)}, u32[]{:S(2)}, u32[]{:S(2)}) %collective-permute-start.24) | collective-permute-done | bytes 36896 | tf_op jit(solution)/shard_map/ppermute | solution.py:36
  51.1 1.2 %collective-permute-done.23 = f32[72,128]{1,0:T(8,128)S(1)} collective-permute-done((f32[72,128]{1,0:T(8,128)S(1)}, f32[72,128]{1,0:T(8,128)S(1)}, u32[]{:S(2)}, u32[]{:S(2)}) %collective-permute-start.23) | collective-permute-done | bytes 36896 | tf_op jit(solution)/shard_map/ppermute | solution.py:36
  52.3 1.3 %collective-permute-start.25 = (f32[72,128]{1,0:T(8,128)S(1)}, f32[72,128]{1,0:T(8,128)S(1)}, u32[]{:S(2)}, u32[]{:S(2)}) collective-permute-start(f32[72,128]{1,0:T(8,128)S(1)} %add_add_fusion), channel_id=1, source_target_pairs={{0,1},{1,0},{2,3},{3,2},{4,5},{5,4},{6,7},{7,6},{8,9},{9,8},{10,11... | collective-permute-start | bytes 110600 | tf_op jit(solution)/shard_map/ppermute | solution.py:18
  53.6 0.9 %collective-permute-done.25 = f32[72,128]{1,0:T(8,128)S(1)} collective-permute-done((f32[72,128]{1,0:T(8,128)S(1)}, f32[72,128]{1,0:T(8,128)S(1)}, u32[]{:S(2)}, u32[]{:S(2)}) %collective-permute-start.25) | collective-permute-done | bytes 36896 | tf_op jit(solution)/shard_map/ppermute | solution.py:18
  54.5 4.1 %make_basis.1 = (f32[512,128]{1,0:T(8,128)}, f32[128,1024]{1,0:T(8,128)S(1)}, f32[128,1024]{1,0:T(8,128)S(1)}, f32[128,1024]{1,0:T(8,128)S(1)}, f32[128,1024]{1,0:T(8,128)S(1)}) custom-call(f32[72,128]{1,0:T(8,128)S(1)} %add.116.gram_ref, f32[128,512]{1,0:T(8,128)S(1)} %get-tuple-element.18.sketch_ref, bf16[512,4096]{1,0:T(8,128)(2,1)} %slab_ref.5), custom_call_target="tpu_custom_call" | custom-call | tf_op jit(solution)/shard_map/make_basis/pallas_call | solution.py:279
  58.7 0.9 %collective-permute-start.26 = (bf16[2,2,16,1024]{3,2,0,1:T(8,128)(2,1)S(1)}, bf16[2,2,16,1024]{3,2,0,1:T(8,128)(2,1)S(1)}, u32[]{:S(2)}, u32[]{:S(2)}) collective-permute-start(bf16[2,2,16,1024]{3,2,0,1:T(8,128)(2,1)S(1)} %fusion.22), channel_id=1, source_target_pairs={{0,2},{2,0},{4,6},{6,4},{8,10},{10,8},{12,14},{14,12},{1,3},{3,1},... | collective-permute-start | bytes 393224 | tf_op jit(solution)/shard_map/ppermute | solution.py:18
  59.6 1.8 %collective-permute-start.29 = (bf16[2,2,16,1024]{3,2,0,1:T(8,128)(2,1)S(1)}, bf16[2,2,16,1024]{3,2,0,1:T(8,128)(2,1)S(1)}, u32[]{:S(2)}, u32[]{:S(2)}) collective-permute-start(bf16[2,2,16,1024]{3,2,0,1:T(8,128)(2,1)S(1)} %fusion.23), channel_id=1, source_target_pairs={{0,4},{2,6},{4,0},{6,2},{8,12},{10,14},{12,8},{14,10},{1,5},{3,7},... | collective-permute-start | bytes 393224 | tf_op jit(solution)/shard_map/ppermute | solution.py:18
  61.5 1.3 %collective-permute-start.32 = (bf16[2,2,16,1024]{3,2,0,1:T(8,128)(2,1)S(1)}, bf16[2,2,16,1024]{3,2,0,1:T(8,128)(2,1)S(1)}, u32[]{:S(2)}, u32[]{:S(2)}) collective-permute-start(bf16[2,2,16,1024]{3,2,0,1:T(8,128)(2,1)S(1)} %fusion.24), channel_id=1, source_target_pairs={{0,2},{2,0},{4,6},{6,4},{8,10},{10,8},{12,14},{14,12},{1,3},{3,1},... | collective-permute-start | bytes 393224 | tf_op jit(solution)/shard_map/ppermute | solution.py:18
  63.2 1.8 %collective-permute-done.26 = bf16[2,2,16,1024]{3,2,0,1:T(8,128)(2,1)S(1)} collective-permute-done((bf16[2,2,16,1024]{3,2,0,1:T(8,128)(2,1)S(1)}, bf16[2,2,16,1024]{3,2,0,1:T(8,128)(2,1)S(1)}, u32[]{:S(2)}, u32[]{:S(2)}) %collective-permute-start.26) | collective-permute-done | bytes 131104 | tf_op jit(solution)/shard_map/ppermute | solution.py:18
  65.0 1.9 %collective-permute-start.27 = (bf16[2,16,1024]{2,1,0:T(8,128)(2,1)S(1)}, bf16[2,16,1024]{2,1,0:T(8,128)(2,1)S(1)}, u32[]{:S(2)}, u32[]{:S(2)}) collective-permute-start(bf16[2,16,1024]{2,1,0:T(8,128)(2,1)S(1)} %fusion.26), channel_id=1, source_target_pairs={{0,4},{2,6},{4,0},{6,2},{8,12},{10,14},{12,8},{14,10},{1,5},{3,7},... | collective-permute-start | bytes 196616 | tf_op jit(solution)/shard_map/ppermute | solution.py:18
  67.0 0.9 %collective-permute-start.30 = (bf16[2,16,1024]{2,1,0:T(8,128)(2,1)S(1)}, bf16[2,16,1024]{2,1,0:T(8,128)(2,1)S(1)}, u32[]{:S(2)}, u32[]{:S(2)}) collective-permute-start(bf16[2,16,1024]{2,1,0:T(8,128)(2,1)S(1)} %fusion.27), channel_id=1, source_target_pairs={{0,2},{2,0},{4,6},{6,4},{8,10},{10,8},{12,14},{14,12},{1,3},{3,1},... | collective-permute-start | bytes 196616 | tf_op jit(solution)/shard_map/ppermute | solution.py:18
  67.9 1.3 %collective-permute-start.33 = (bf16[2,16,1024]{2,1,0:T(8,128)(2,1)S(1)}, bf16[2,16,1024]{2,1,0:T(8,128)(2,1)S(1)}, u32[]{:S(2)}, u32[]{:S(2)}) collective-permute-start(bf16[2,16,1024]{2,1,0:T(8,128)(2,1)S(1)} %fusion.28), channel_id=1, source_target_pairs={{0,4},{2,6},{4,0},{6,2},{8,12},{10,14},{12,8},{14,10},{1,5},{3,7},... | collective-permute-start | bytes 196616 | tf_op jit(solution)/shard_map/ppermute | solution.py:18
  69.3 0.9 %collective-permute-start.36 = (bf16[2,16,1024]{2,1,0:T(8,128)(2,1)S(1)}, bf16[2,16,1024]{2,1,0:T(8,128)(2,1)S(1)}, u32[]{:S(2)}, u32[]{:S(2)}) collective-permute-start(bf16[2,16,1024]{2,1,0:T(8,128)(2,1)S(1)} %fusion.29), channel_id=1, source_target_pairs={{0,2},{2,0},{4,6},{6,4},{8,10},{10,8},{12,14},{14,12},{1,3},{3,1},... | collective-permute-start | bytes 196616 | tf_op jit(solution)/shard_map/ppermute | solution.py:18
  70.2 1.9 %collective-permute-start.28 = (bf16[16,1024]{1,0:T(8,128)(2,1)S(1)}, bf16[16,1024]{1,0:T(8,128)(2,1)S(1)}, u32[]{:S(2)}, u32[]{:S(2)}) collective-permute-start(bf16[16,1024]{1,0:T(8,128)(2,1)S(1)} %fusion.34), channel_id=1, source_target_pairs={{0,8},{2,10},{4,12},{6,14},{8,0},{10,2},{12,4},{14,6},{1,9},{3,11}... | collective-permute-start | bytes 98312 | tf_op jit(solution)/shard_map/ppermute | solution.py:18
  72.2 1.2 %collective-permute-start.31 = (bf16[16,1024]{1,0:T(8,128)(2,1)S(1)}, bf16[16,1024]{1,0:T(8,128)(2,1)S(1)}, u32[]{:S(2)}, u32[]{:S(2)}) collective-permute-start(bf16[16,1024]{1,0:T(8,128)(2,1)S(1)} %fusion.35), channel_id=1, source_target_pairs={{0,8},{2,10},{4,12},{6,14},{8,0},{10,2},{12,4},{14,6},{1,9},{3,11}... | collective-permute-start | bytes 98312 | tf_op jit(solution)/shard_map/ppermute | solution.py:18
  73.4 1.8 %collective-permute-start.34 = (bf16[16,1024]{1,0:T(8,128)(2,1)S(1)}, bf16[16,1024]{1,0:T(8,128)(2,1)S(1)}, u32[]{:S(2)}, u32[]{:S(2)}) collective-permute-start(bf16[16,1024]{1,0:T(8,128)(2,1)S(1)} %fusion.36), channel_id=1, source_target_pairs={{0,8},{2,10},{4,12},{6,14},{8,0},{10,2},{12,4},{14,6},{1,9},{3,11}... | collective-permute-start | bytes 98312 | tf_op jit(solution)/shard_map/ppermute | solution.py:18
  75.3 1.2 %collective-permute-start.37 = (bf16[16,1024]{1,0:T(8,128)(2,1)S(1)}, bf16[16,1024]{1,0:T(8,128)(2,1)S(1)}, u32[]{:S(2)}, u32[]{:S(2)}) collective-permute-start(bf16[16,1024]{1,0:T(8,128)(2,1)S(1)} %fusion.37), channel_id=1, source_target_pairs={{0,8},{2,10},{4,12},{6,14},{8,0},{10,2},{12,4},{14,6},{1,9},{3,11}... | collective-permute-start | bytes 98312 | tf_op jit(solution)/shard_map/ppermute | solution.py:18
  76.5 1.3 %collective-permute-done.31 = bf16[16,1024]{1,0:T(8,128)(2,1)S(1)} collective-permute-done((bf16[16,1024]{1,0:T(8,128)(2,1)S(1)}, bf16[16,1024]{1,0:T(8,128)(2,1)S(1)}, u32[]{:S(2)}, u32[]{:S(2)}) %collective-permute-start.31) | collective-permute-done | bytes 32800 | tf_op jit(solution)/shard_map/ppermute | solution.py:18
  78.5 2.1 %collective-permute-done.37 = bf16[16,1024]{1,0:T(8,128)(2,1)S(1)} collective-permute-done((bf16[16,1024]{1,0:T(8,128)(2,1)S(1)}, bf16[16,1024]{1,0:T(8,128)(2,1)S(1)}, u32[]{:S(2)}, u32[]{:S(2)}) %collective-permute-start.37) | collective-permute-done | bytes 32800 | tf_op jit(solution)/shard_map/ppermute | solution.py:18
  80.5 0.7 pad_maximum_fusion
  (105 shorter events, 7.7 us)
Async XLA Ops:
  0.6 0.9 %copy-start = (bf16[512,128]{1,0:T(8,128)(2,1)S(1)}, bf16[512,128]{1,0:T(8,128)(2,1)}, u32[]{:S(2)}) copy-start(bf16[512,128]{1,0:T(8,128)(2,1)} %start_ref.3) | copy-start | bytes 393220
  1.6 6.6 %copy-start.1 = (bf16[512,128]{1,0:T(8,128)(2,1)S(1)}, bf16[512,128]{1,0:T(8,128)(2,1)}, u32[]{:S(2)}) copy-start(bf16[512,128]{1,0:T(8,128)(2,1)} %start_ref.3) | copy-start | bytes 393220
  3.5 7.3 %collective-permute-start.15 = (bf16[128,512]{1,0:T(8,128)(2,1)S(1)}, bf16[128,512]{1,0:T(8,128)(2,1)S(1)}, u32[]{:S(2)}, u32[]{:S(2)}) collective-permute-start(bf16[128,512]{1,0:T(8,128)(2,1)S(1)} %select_convert_fusion.4), channel_id=1, source_target_pairs={{0,4},{2,6},{4,0},{6,2},{8,12},{10,14},{12,8},{14,10},{1,5},{3,7},... | collective-permute-start | bytes 393224 | tf_op jit(solution)/shard_map/ppermute | solution.py:18
  6.6 6.3 %collective-permute-start.10 = (bf16[128,512]{1,0:T(8,128)(2,1)S(1)}, bf16[128,512]{1,0:T(8,128)(2,1)S(1)}, u32[]{:S(2)}, u32[]{:S(2)}) collective-permute-start(bf16[128,512]{1,0:T(8,128)(2,1)S(1)} %select_convert_fusion.5), channel_id=1, source_target_pairs={{0,2},{2,0},{4,6},{6,4},{8,10},{10,8},{12,14},{14,12},{1,3},{3,1},... | collective-permute-start | bytes 393224 | tf_op jit(solution)/shard_map/ppermute | solution.py:18
  10.1 5.7 %collective-permute-start.5 = (bf16[128,512]{1,0:T(8,128)(2,1)S(1)}, bf16[128,512]{1,0:T(8,128)(2,1)S(1)}, u32[]{:S(2)}, u32[]{:S(2)}) collective-permute-start(bf16[128,512]{1,0:T(8,128)(2,1)S(1)} %select_convert_fusion.6), channel_id=1, source_target_pairs={{0,4},{2,6},{4,0},{6,2},{8,12},{10,14},{12,8},{14,10},{1,5},{3,7},... | collective-permute-start | bytes 393224 | tf_op jit(solution)/shard_map/ppermute | solution.py:18
  10.6 5.9 %collective-permute-start = (bf16[128,512]{1,0:T(8,128)(2,1)S(1)}, bf16[128,512]{1,0:T(8,128)(2,1)S(1)}, u32[]{:S(2)}, u32[]{:S(2)}) collective-permute-start(bf16[128,512]{1,0:T(8,128)(2,1)S(1)} %select_convert_fusion.7), channel_id=1, source_target_pairs={{0,2},{2,0},{4,6},{6,4},{8,10},{10,8},{12,14},{14,12},{1,3},{3,1},... | collective-permute-start | bytes 393224 | tf_op jit(solution)/shard_map/ppermute | solution.py:18
  10.9 7.3 %collective-permute-start.16 = (bf16[128,256]{1,0:T(8,128)(2,1)S(1)}, bf16[128,256]{1,0:T(8,128)(2,1)S(1)}, u32[]{:S(2)}, u32[]{:S(2)}) collective-permute-start(bf16[128,256]{1,0:T(8,128)(2,1)S(1)} %select_convert_fusion.12), channel_id=1, source_target_pairs={{0,2},{2,0},{4,6},{6,4},{8,10},{10,8},{12,14},{14,12},{1,3},{3,1},... | collective-permute-start | bytes 196616 | tf_op jit(solution)/shard_map/ppermute | solution.py:18
  12.9 25.9 %copy-start.2 = (bf16[512,4096]{1,0:T(8,128)(2,1)S(1)}, bf16[512,4096]{1,0:T(8,128)(2,1)}, u32[]{:S(2)}) copy-start(bf16[512,4096]{1,0:T(8,128)(2,1)} %slab_ref.5) | copy-start | bytes 12582916
  13.0 8.0 %collective-permute-start.11 = (bf16[128,256]{1,0:T(8,128)(2,1)S(1)}, bf16[128,256]{1,0:T(8,128)(2,1)S(1)}, u32[]{:S(2)}, u32[]{:S(2)}) collective-permute-start(bf16[128,256]{1,0:T(8,128)(2,1)S(1)} %select_convert_fusion.13), channel_id=1, source_target_pairs={{0,4},{2,6},{4,0},{6,2},{8,12},{10,14},{12,8},{14,10},{1,5},{3,7},... | collective-permute-start | bytes 196616 | tf_op jit(solution)/shard_map/ppermute | solution.py:18
  15.9 5.4 %collective-permute-start.6 = (bf16[128,256]{1,0:T(8,128)(2,1)S(1)}, bf16[128,256]{1,0:T(8,128)(2,1)S(1)}, u32[]{:S(2)}, u32[]{:S(2)}) collective-permute-start(bf16[128,256]{1,0:T(8,128)(2,1)S(1)} %select_convert_fusion.14), channel_id=1, source_target_pairs={{0,2},{2,0},{4,6},{6,4},{8,10},{10,8},{12,14},{14,12},{1,3},{3,1},... | collective-permute-start | bytes 196616 | tf_op jit(solution)/shard_map/ppermute | solution.py:18
  16.6 7.4 %collective-permute-start.1 = (bf16[128,256]{1,0:T(8,128)(2,1)S(1)}, bf16[128,256]{1,0:T(8,128)(2,1)S(1)}, u32[]{:S(2)}, u32[]{:S(2)}) collective-permute-start(bf16[128,256]{1,0:T(8,128)(2,1)S(1)} %select_convert_fusion.15), channel_id=1, source_target_pairs={{0,4},{2,6},{4,0},{6,2},{8,12},{10,14},{12,8},{14,10},{1,5},{3,7},... | collective-permute-start | bytes 196616 | tf_op jit(solution)/shard_map/ppermute | solution.py:18
  18.3 8.6 %collective-permute-start.17 = (bf16[128,256]{1,0:T(8,128)(2,1)S(1)}, bf16[128,256]{1,0:T(8,128)(2,1)S(1)}, u32[]{:S(2)}, u32[]{:S(2)}) collective-permute-start(bf16[128,256]{1,0:T(8,128)(2,1)S(1)} %fusion.41), channel_id=1, source_target_pairs={{0,8},{2,10},{4,12},{6,14},{8,0},{10,2},{12,4},{14,6},{1,9},{3,11}... | collective-permute-start | bytes 196616 | tf_op jit(solution)/shard_map/ppermute | solution.py:18
  21.0 8.7 %collective-permute-start.12 = (bf16[128,256]{1,0:T(8,128)(2,1)S(1)}, bf16[128,256]{1,0:T(8,128)(2,1)S(1)}, u32[]{:S(2)}, u32[]{:S(2)}) collective-permute-start(bf16[128,256]{1,0:T(8,128)(2,1)S(1)} %fusion.40), channel_id=1, source_target_pairs={{0,8},{2,10},{4,12},{6,14},{8,0},{10,2},{12,4},{14,6},{1,9},{3,11}... | collective-permute-start | bytes 196616 | tf_op jit(solution)/shard_map/ppermute | solution.py:18
  21.4 9.0 %collective-permute-start.7 = (bf16[128,256]{1,0:T(8,128)(2,1)S(1)}, bf16[128,256]{1,0:T(8,128)(2,1)S(1)}, u32[]{:S(2)}, u32[]{:S(2)}) collective-permute-start(bf16[128,256]{1,0:T(8,128)(2,1)S(1)} %fusion.39), channel_id=1, source_target_pairs={{0,8},{2,10},{4,12},{6,14},{8,0},{10,2},{12,4},{14,6},{1,9},{3,11}... | collective-permute-start | bytes 196616 | tf_op jit(solution)/shard_map/ppermute | solution.py:18
  24.1 7.0 %collective-permute-start.2 = (bf16[128,256]{1,0:T(8,128)(2,1)S(1)}, bf16[128,256]{1,0:T(8,128)(2,1)S(1)}, u32[]{:S(2)}, u32[]{:S(2)}) collective-permute-start(bf16[128,256]{1,0:T(8,128)(2,1)S(1)} %fusion.38), channel_id=1, source_target_pairs={{0,8},{2,10},{4,12},{6,14},{8,0},{10,2},{12,4},{14,6},{1,9},{3,11}... | collective-permute-start | bytes 196616 | tf_op jit(solution)/shard_map/ppermute | solution.py:18
  26.9 5.2 %collective-permute-start.18 = (bf16[128,256]{1,0:T(8,128)(2,1)S(1)}, bf16[128,256]{1,0:T(8,128)(2,1)S(1)}, u32[]{:S(2)}, u32[]{:S(2)}) collective-permute-start(bf16[128,256]{1,0:T(8,128)(2,1)S(1)} %multiply_convert_fusion), channel_id=1, source_target_pairs={{0,2},{2,0},{4,6},{6,4},{8,10},{10,8},{12,14},{14,12},{1,3},{3,1},... | collective-permute-start | bytes 196616 | tf_op jit(solution)/shard_map/ppermute | solution.py:18
  29.7 5.0 %collective-permute-start.13 = (bf16[128,256]{1,0:T(8,128)(2,1)S(1)}, bf16[128,256]{1,0:T(8,128)(2,1)S(1)}, u32[]{:S(2)}, u32[]{:S(2)}) collective-permute-start(bf16[128,256]{1,0:T(8,128)(2,1)S(1)} %multiply_convert_fusion.1), channel_id=1, source_target_pairs={{0,4},{2,6},{4,0},{6,2},{8,12},{10,14},{12,8},{14,10},{1,5},{3,7},... | collective-permute-start | bytes 196616 | tf_op jit(solution)/shard_map/ppermute | solution.py:18
  30.4 4.9 %collective-permute-start.8 = (bf16[128,256]{1,0:T(8,128)(2,1)S(1)}, bf16[128,256]{1,0:T(8,128)(2,1)S(1)}, u32[]{:S(2)}, u32[]{:S(2)}) collective-permute-start(bf16[128,256]{1,0:T(8,128)(2,1)S(1)} %multiply_convert_fusion.2), channel_id=1, source_target_pairs={{0,2},{2,0},{4,6},{6,4},{8,10},{10,8},{12,14},{14,12},{1,3},{3,1},... | collective-permute-start | bytes 196616 | tf_op jit(solution)/shard_map/ppermute | solution.py:18
  31.1 5.6 %collective-permute-start.3 = (bf16[128,256]{1,0:T(8,128)(2,1)S(1)}, bf16[128,256]{1,0:T(8,128)(2,1)S(1)}, u32[]{:S(2)}, u32[]{:S(2)}) collective-permute-start(bf16[128,256]{1,0:T(8,128)(2,1)S(1)} %multiply_convert_fusion.3), channel_id=1, source_target_pairs={{0,4},{2,6},{4,0},{6,2},{8,12},{10,14},{12,8},{14,10},{1,5},{3,7},... | collective-permute-start | bytes 196616 | tf_op jit(solution)/shard_map/ppermute | solution.py:18
  32.1 6.8 %collective-permute-start.19 = (bf16[128,512]{1,0:T(8,128)(2,1)S(1)}, bf16[128,512]{1,0:T(8,128)(2,1)S(1)}, u32[]{:S(2)}, u32[]{:S(2)}) collective-permute-start(bf16[128,512]{1,0:T(8,128)(2,1)S(1)} %pad_maximum_fusion.4), channel_id=1, source_target_pairs={{0,4},{2,6},{4,0},{6,2},{8,12},{10,14},{12,8},{14,10},{1,5},{3,7},... | collective-permute-start | bytes 393224 | tf_op jit(solution)/shard_map/ppermute | solution.py:18
  34.7 5.0 %collective-permute-start.14 = (bf16[128,512]{1,0:T(8,128)(2,1)S(1)}, bf16[128,512]{1,0:T(8,128)(2,1)S(1)}, u32[]{:S(2)}, u32[]{:S(2)}) collective-permute-start(bf16[128,512]{1,0:T(8,128)(2,1)S(1)} %pad_maximum_fusion.3), channel_id=1, source_target_pairs={{0,2},{2,0},{4,6},{6,4},{8,10},{10,8},{12,14},{14,12},{1,3},{3,1},... | collective-permute-start | bytes 393224 | tf_op jit(solution)/shard_map/ppermute | solution.py:18
  35.4 5.0 %collective-permute-start.9 = (bf16[128,512]{1,0:T(8,128)(2,1)S(1)}, bf16[128,512]{1,0:T(8,128)(2,1)S(1)}, u32[]{:S(2)}, u32[]{:S(2)}) collective-permute-start(bf16[128,512]{1,0:T(8,128)(2,1)S(1)} %pad_maximum_fusion.2), channel_id=1, source_target_pairs={{0,4},{2,6},{4,0},{6,2},{8,12},{10,14},{12,8},{14,10},{1,5},{3,7},... | collective-permute-start | bytes 393224 | tf_op jit(solution)/shard_map/ppermute | solution.py:18
  36.8 5.0 %collective-permute-start.4 = (bf16[128,512]{1,0:T(8,128)(2,1)S(1)}, bf16[128,512]{1,0:T(8,128)(2,1)S(1)}, u32[]{:S(2)}, u32[]{:S(2)}) collective-permute-start(bf16[128,512]{1,0:T(8,128)(2,1)S(1)} %pad_maximum_fusion.1), channel_id=1, source_target_pairs={{0,2},{2,0},{4,6},{6,4},{8,10},{10,8},{12,14},{14,12},{1,3},{3,1},... | collective-permute-start | bytes 393224 | tf_op jit(solution)/shard_map/ppermute | solution.py:18
  42.3 1.6 %collective-permute-start.20 = (f32[512,128]{1,0:T(8,128)S(1)}, f32[512,128]{1,0:T(8,128)S(1)}, u32[]{:S(2)}, u32[]{:S(2)}) collective-permute-start(f32[512,128]{1,0:T(8,128)S(1)} %fusion.2.mine_ref), channel_id=1, source_target_pairs={{0,1},{1,0},{2,3},{3,2},{4,5},{5,4},{6,7},{7,6},{8,9},{9,8},{10,11... | collective-permute-start | bytes 786440 | tf_op jit(solution)/shard_map/ppermute | solution.py:18
  44.5 6.6 %collective-permute-start.24 = (f32[72,128]{1,0:T(8,128)S(1)}, f32[72,128]{1,0:T(8,128)S(1)}, u32[]{:S(2)}, u32[]{:S(2)}) collective-permute-start(f32[72,128]{1,0:T(8,128)S(1)} %get-tuple-element.17), channel_id=1, source_target_pairs={{0,10},{1,15},{2,8},{3,13},{4,14},{5,11},{6,12},{7,9},{8,2},{9,7},... | collective-permute-start | bytes 110600 | tf_op jit(solution)/shard_map/ppermute | solution.py:36
  46.7 5.5 %collective-permute-start.23 = (f32[72,128]{1,0:T(8,128)S(1)}, f32[72,128]{1,0:T(8,128)S(1)}, u32[]{:S(2)}, u32[]{:S(2)}) collective-permute-start(f32[72,128]{1,0:T(8,128)S(1)} %get-tuple-element.17), channel_id=1, source_target_pairs={{0,8},{1,13},{2,10},{3,15},{4,12},{5,9},{6,14},{7,11},{8,0},{9,5},... | collective-permute-start | bytes 110600 | tf_op jit(solution)/shard_map/ppermute | solution.py:36
  47.7 4.5 %collective-permute-start.22 = (f32[72,128]{1,0:T(8,128)S(1)}, f32[72,128]{1,0:T(8,128)S(1)}, u32[]{:S(2)}, u32[]{:S(2)}) collective-permute-start(f32[72,128]{1,0:T(8,128)S(1)} %get-tuple-element.17), channel_id=1, source_target_pairs={{0,2},{1,7},{2,0},{3,5},{4,6},{5,3},{6,4},{7,1},{8,10},{9,15},{10,... | collective-permute-start | bytes 110600 | tf_op jit(solution)/shard_map/ppermute | solution.py:36
  48.9 3.3 %collective-permute-start.21 = (f32[72,128]{1,0:T(8,128)S(1)}, f32[72,128]{1,0:T(8,128)S(1)}, u32[]{:S(2)}, u32[]{:S(2)}) collective-permute-start(f32[72,128]{1,0:T(8,128)S(1)} %get-tuple-element.17), channel_id=1, source_target_pairs={{1,5},{3,7},{5,1},{7,3},{9,13},{11,15},{13,9},{15,11},{17,21},{19,... | collective-permute-start | bytes 110600 | tf_op jit(solution)/shard_map/ppermute | solution.py:36
  52.3 2.2 %collective-permute-start.25 = (f32[72,128]{1,0:T(8,128)S(1)}, f32[72,128]{1,0:T(8,128)S(1)}, u32[]{:S(2)}, u32[]{:S(2)}) collective-permute-start(f32[72,128]{1,0:T(8,128)S(1)} %add_add_fusion), channel_id=1, source_target_pairs={{0,1},{1,0},{2,3},{3,2},{4,5},{5,4},{6,7},{7,6},{8,9},{9,8},{10,11... | collective-permute-start | bytes 110600 | tf_op jit(solution)/shard_map/ppermute | solution.py:18
  58.7 6.3 %collective-permute-start.26 = (bf16[2,2,16,1024]{3,2,0,1:T(8,128)(2,1)S(1)}, bf16[2,2,16,1024]{3,2,0,1:T(8,128)(2,1)S(1)}, u32[]{:S(2)}, u32[]{:S(2)}) collective-permute-start(bf16[2,2,16,1024]{3,2,0,1:T(8,128)(2,1)S(1)} %fusion.22), channel_id=1, source_target_pairs={{0,2},{2,0},{4,6},{6,4},{8,10},{10,8},{12,14},{14,12},{1,3},{3,1},... | collective-permute-start | bytes 393224 | tf_op jit(solution)/shard_map/ppermute | solution.py:18
  59.6 7.3 %collective-permute-start.29 = (bf16[2,2,16,1024]{3,2,0,1:T(8,128)(2,1)S(1)}, bf16[2,2,16,1024]{3,2,0,1:T(8,128)(2,1)S(1)}, u32[]{:S(2)}, u32[]{:S(2)}) collective-permute-start(bf16[2,2,16,1024]{3,2,0,1:T(8,128)(2,1)S(1)} %fusion.23), channel_id=1, source_target_pairs={{0,4},{2,6},{4,0},{6,2},{8,12},{10,14},{12,8},{14,10},{1,5},{3,7},... | collective-permute-start | bytes 393224 | tf_op jit(solution)/shard_map/ppermute | solution.py:18
  61.5 6.4 %collective-permute-start.32 = (bf16[2,2,16,1024]{3,2,0,1:T(8,128)(2,1)S(1)}, bf16[2,2,16,1024]{3,2,0,1:T(8,128)(2,1)S(1)}, u32[]{:S(2)}, u32[]{:S(2)}) collective-permute-start(bf16[2,2,16,1024]{3,2,0,1:T(8,128)(2,1)S(1)} %fusion.24), channel_id=1, source_target_pairs={{0,2},{2,0},{4,6},{6,4},{8,10},{10,8},{12,14},{14,12},{1,3},{3,1},... | collective-permute-start | bytes 393224 | tf_op jit(solution)/shard_map/ppermute | solution.py:18
  62.8 6.4 %collective-permute-start.35 = (bf16[2,2,16,1024]{3,2,0,1:T(8,128)(2,1)S(1)}, bf16[2,2,16,1024]{3,2,0,1:T(8,128)(2,1)S(1)}, u32[]{:S(2)}, u32[]{:S(2)}) collective-permute-start(bf16[2,2,16,1024]{3,2,0,1:T(8,128)(2,1)S(1)} %fusion.25), channel_id=1, source_target_pairs={{0,4},{2,6},{4,0},{6,2},{8,12},{10,14},{12,8},{14,10},{1,5},{3,7},... | collective-permute-start | bytes 393224 | tf_op jit(solution)/shard_map/ppermute | solution.py:18
  65.0 5.2 %collective-permute-start.27 = (bf16[2,16,1024]{2,1,0:T(8,128)(2,1)S(1)}, bf16[2,16,1024]{2,1,0:T(8,128)(2,1)S(1)}, u32[]{:S(2)}, u32[]{:S(2)}) collective-permute-start(bf16[2,16,1024]{2,1,0:T(8,128)(2,1)S(1)} %fusion.26), channel_id=1, source_target_pairs={{0,4},{2,6},{4,0},{6,2},{8,12},{10,14},{12,8},{14,10},{1,5},{3,7},... | collective-permute-start | bytes 196616 | tf_op jit(solution)/shard_map/ppermute | solution.py:18
  67.0 5.1 %collective-permute-start.30 = (bf16[2,16,1024]{2,1,0:T(8,128)(2,1)S(1)}, bf16[2,16,1024]{2,1,0:T(8,128)(2,1)S(1)}, u32[]{:S(2)}, u32[]{:S(2)}) collective-permute-start(bf16[2,16,1024]{2,1,0:T(8,128)(2,1)S(1)} %fusion.27), channel_id=1, source_target_pairs={{0,2},{2,0},{4,6},{6,4},{8,10},{10,8},{12,14},{14,12},{1,3},{3,1},... | collective-permute-start | bytes 196616 | tf_op jit(solution)/shard_map/ppermute | solution.py:18
  67.9 5.4 %collective-permute-start.33 = (bf16[2,16,1024]{2,1,0:T(8,128)(2,1)S(1)}, bf16[2,16,1024]{2,1,0:T(8,128)(2,1)S(1)}, u32[]{:S(2)}, u32[]{:S(2)}) collective-permute-start(bf16[2,16,1024]{2,1,0:T(8,128)(2,1)S(1)} %fusion.28), channel_id=1, source_target_pairs={{0,4},{2,6},{4,0},{6,2},{8,12},{10,14},{12,8},{14,10},{1,5},{3,7},... | collective-permute-start | bytes 196616 | tf_op jit(solution)/shard_map/ppermute | solution.py:18
  69.3 5.9 %collective-permute-start.36 = (bf16[2,16,1024]{2,1,0:T(8,128)(2,1)S(1)}, bf16[2,16,1024]{2,1,0:T(8,128)(2,1)S(1)}, u32[]{:S(2)}, u32[]{:S(2)}) collective-permute-start(bf16[2,16,1024]{2,1,0:T(8,128)(2,1)S(1)} %fusion.29), channel_id=1, source_target_pairs={{0,2},{2,0},{4,6},{6,4},{8,10},{10,8},{12,14},{14,12},{1,3},{3,1},... | collective-permute-start | bytes 196616 | tf_op jit(solution)/shard_map/ppermute | solution.py:18
  70.2 6.3 %collective-permute-start.28 = (bf16[16,1024]{1,0:T(8,128)(2,1)S(1)}, bf16[16,1024]{1,0:T(8,128)(2,1)S(1)}, u32[]{:S(2)}, u32[]{:S(2)}) collective-permute-start(bf16[16,1024]{1,0:T(8,128)(2,1)S(1)} %fusion.34), channel_id=1, source_target_pairs={{0,8},{2,10},{4,12},{6,14},{8,0},{10,2},{12,4},{14,6},{1,9},{3,11}... | collective-permute-start | bytes 98312 | tf_op jit(solution)/shard_map/ppermute | solution.py:18
  72.2 5.7 %collective-permute-start.31 = (bf16[16,1024]{1,0:T(8,128)(2,1)S(1)}, bf16[16,1024]{1,0:T(8,128)(2,1)S(1)}, u32[]{:S(2)}, u32[]{:S(2)}) collective-permute-start(bf16[16,1024]{1,0:T(8,128)(2,1)S(1)} %fusion.35), channel_id=1, source_target_pairs={{0,8},{2,10},{4,12},{6,14},{8,0},{10,2},{12,4},{14,6},{1,9},{3,11}... | collective-permute-start | bytes 98312 | tf_op jit(solution)/shard_map/ppermute | solution.py:18
  73.4 5.0 %collective-permute-start.34 = (bf16[16,1024]{1,0:T(8,128)(2,1)S(1)}, bf16[16,1024]{1,0:T(8,128)(2,1)S(1)}, u32[]{:S(2)}, u32[]{:S(2)}) collective-permute-start(bf16[16,1024]{1,0:T(8,128)(2,1)S(1)} %fusion.36), channel_id=1, source_target_pairs={{0,8},{2,10},{4,12},{6,14},{8,0},{10,2},{12,4},{14,6},{1,9},{3,11}... | collective-permute-start | bytes 98312 | tf_op jit(solution)/shard_map/ppermute | solution.py:18
  75.3 5.2 %collective-permute-start.37 = (bf16[16,1024]{1,0:T(8,128)(2,1)S(1)}, bf16[16,1024]{1,0:T(8,128)(2,1)S(1)}, u32[]{:S(2)}, u32[]{:S(2)}) collective-permute-start(bf16[16,1024]{1,0:T(8,128)(2,1)S(1)} %fusion.37), channel_id=1, source_target_pairs={{0,8},{2,10},{4,12},{6,14},{8,0},{10,2},{12,4},{14,6},{1,9},{3,11}... | collective-permute-start | bytes 98312 | tf_op jit(solution)/shard_map/ppermute | solution.py:18

commit v33 on v32

--- a/solution.py
+++ b/solution.py
@@ -312,7 +312,7 @@
     step = cols_here // CHUNKS
     for c in range(CHUNKS):
         span = slice(c * step, (c + 1) * step)
-        shared = sum_and_share(local_cols[c], "row", orders[c % 2], 1.0 / root_rows)
+        shared = sum_and_share(local_cols[c], "row", orders[1 - c % 2], 1.0 / root_rows)
         partial_sketch = partial_sketch + lax.dot_general(
             activations[:, span],
             shared,

time: 81.5 us -> 81.5 us (level)
  transfers between devices with their start and end apart: 38 -> 38, of which waited for: 19 -> 20; matrix products, arithmetic and copies ran while one was open for 3% -> 3% of each run, Pallas kernels for 2% -> 2%
where the time goes in v33:
time: 81.5 us; the launch traced here: 81.2 us
  starting transfers between devices  44 us (54%)
  waiting for transfers between devices  22.8 us (28%)
  Pallas kernels  8.4 us (10%)
  other arithmetic  2.11 us (3%)
  matrix products  1.76 us (2%)
  between operations  1.11 us (1%)
  local copies, waits for them, and re-layouts  1.05 us (1%)
    ppermute x34, starting transfers between devices, swap(): return lax.ppermute(value, axis, [(i, i ^ distance) for i in range(size)])  38.9 us
    ppermute x34, waiting for transfers between devices, swap(): return lax.ppermute(value, axis, [(i, i ^ distance) for i in range(size)])  20.4 us
    ppermute x4, starting transfers between devices, row_sum(): terms.append(lax.ppermute(value, ('row', 'col'), pairs))  5.1 us
    pallas_call x1, Pallas kernels, make_basis(): pl.pallas_call(functools.partial(basis_kernel, root_rows), out_shape=[jax...  4.1 us
    pallas_call x2, Pallas kernels, first_product(): pl.pallas_call(functools.partial(sketch_kernel, begin), out_shape=[jax.Sh...  3.8 us
    ppermute x4, waiting for transfers between devices, row_sum(): terms.append(lax.ppermute(value, ('row', 'col'), pairs))  2.36 us
    dot_general x4, matrix products, per_device(): lax.dot_general(activations[:, span], shared, (((1,), (1,)), ((), ())), p...  1.76 us
  transfers between devices with their start and end apart: 38, of which 20 were waited for; matrix products, arithmetic and copies ran while one was open for 3% of the time, Pallas kernels for 2%

profile of v33, /device:TPU:0, one launch (start us, length us, event | category | flops | bytes accessed | tf_op | source)
XLA Modules:
  0.0 81.2 jit_solution(16973725892665843090)
XLA Ops:
  0.6 0.9 %copy-done = bf16[512,128]{1,0:T(8,128)(2,1)S(1)} copy-done((bf16[512,128]{1,0:T(8,128)(2,1)S(1)}, bf16[512,128]{1,0:T(8,128)(2,1)}, u32[]{:S(2)}) %copy-start) | copy-done | bytes 131096
  1.5 1.9 %first_product.3 = (f32[128,1024]{1,0:T(8,128)S(1)}, f32[128,1024]{1,0:T(8,128)S(1)}) custom-call(bf16[512,128]{1,0:T(8,128)(2,1)S(1)} %copy-done, bf16[512,4096]{1,0:T(8,128)(2,1)} %slab_ref.5), custom_call_target="tpu_custom_call" | custom-call | flops 268435456 | bytes 2097152 | tf_op jit(solution)/shard_map/first_product/pallas_call | solution.py:117
  3.5 3.0 %collective-permute-start.15 = (bf16[128,512]{1,0:T(8,128)(2,1)S(1)}, bf16[128,512]{1,0:T(8,128)(2,1)S(1)}, u32[]{:S(2)}, u32[]{:S(2)}) collective-permute-start(bf16[128,512]{1,0:T(8,128)(2,1)S(1)} %select_convert_fusion.4), channel_id=1, source_target_pairs={{0,2},{2,0},{4,6},{6,4},{8,10},{10,8},{12,14},{14,12},{1,3},{3,1},... | collective-permute-start | bytes 393224 | tf_op jit(solution)/shard_map/ppermute | solution.py:18
  6.5 1.6 %collective-permute-start.10 = (bf16[128,512]{1,0:T(8,128)(2,1)S(1)}, bf16[128,512]{1,0:T(8,128)(2,1)S(1)}, u32[]{:S(2)}, u32[]{:S(2)}) collective-permute-start(bf16[128,512]{1,0:T(8,128)(2,1)S(1)} %select_convert_fusion.5), channel_id=1, source_target_pairs={{0,4},{2,6},{4,0},{6,2},{8,12},{10,14},{12,8},{14,10},{1,5},{3,7},... | collective-permute-start | bytes 393224 | tf_op jit(solution)/shard_map/ppermute | solution.py:18
  8.2 1.9 %first_product.2 = (f32[128,1024]{1,0:T(8,128)S(1)}, f32[128,1024]{1,0:T(8,128)S(1)}) custom-call(bf16[512,128]{1,0:T(8,128)(2,1)S(1)} %copy-done.1, bf16[512,4096]{1,0:T(8,128)(2,1)} %slab_ref.5), custom_call_target="tpu_custom_call" | custom-call | flops 268435456 | bytes 2097152 | tf_op jit(solution)/shard_map/first_product/pallas_call | solution.py:117
  10.1 0.6 collective-permute-start.5
  10.9 2.1 %collective-permute-start.16 = (bf16[128,256]{1,0:T(8,128)(2,1)S(1)}, bf16[128,256]{1,0:T(8,128)(2,1)S(1)}, u32[]{:S(2)}, u32[]{:S(2)}) collective-permute-start(bf16[128,256]{1,0:T(8,128)(2,1)S(1)} %select_convert_fusion.12), channel_id=1, source_target_pairs={{0,4},{2,6},{4,0},{6,2},{8,12},{10,14},{12,8},{14,10},{1,5},{3,7},... | collective-permute-start | bytes 196616 | tf_op jit(solution)/shard_map/ppermute | solution.py:18
  13.0 1.6 %collective-permute-start.11 = (bf16[128,256]{1,0:T(8,128)(2,1)S(1)}, bf16[128,256]{1,0:T(8,128)(2,1)S(1)}, u32[]{:S(2)}, u32[]{:S(2)}) collective-permute-start(bf16[128,256]{1,0:T(8,128)(2,1)S(1)} %select_convert_fusion.13), channel_id=1, source_target_pairs={{0,2},{2,0},{4,6},{6,4},{8,10},{10,8},{12,14},{14,12},{1,3},{3,1},... | collective-permute-start | bytes 196616 | tf_op jit(solution)/shard_map/ppermute | solution.py:18
  14.6 1.2 %collective-permute-done.5 = bf16[128,512]{1,0:T(8,128)(2,1)S(1)} collective-permute-done((bf16[128,512]{1,0:T(8,128)(2,1)S(1)}, bf16[128,512]{1,0:T(8,128)(2,1)S(1)}, u32[]{:S(2)}, u32[]{:S(2)}) %collective-permute-start.5) | collective-permute-done | bytes 131104 | tf_op jit(solution)/shard_map/ppermute | solution.py:18
  16.5 1.7 %collective-permute-start.1 = (bf16[128,256]{1,0:T(8,128)(2,1)S(1)}, bf16[128,256]{1,0:T(8,128)(2,1)S(1)}, u32[]{:S(2)}, u32[]{:S(2)}) collective-permute-start(bf16[128,256]{1,0:T(8,128)(2,1)S(1)} %select_convert_fusion.15), channel_id=1, source_target_pairs={{0,2},{2,0},{4,6},{6,4},{8,10},{10,8},{12,14},{14,12},{1,3},{3,1},... | collective-permute-start | bytes 196616 | tf_op jit(solution)/shard_map/ppermute | solution.py:18
  18.2 2.7 %collective-permute-start.17 = (bf16[128,256]{1,0:T(8,128)(2,1)S(1)}, bf16[128,256]{1,0:T(8,128)(2,1)S(1)}, u32[]{:S(2)}, u32[]{:S(2)}) collective-permute-start(bf16[128,256]{1,0:T(8,128)(2,1)S(1)} %fusion.41), channel_id=1, source_target_pairs={{0,8},{2,10},{4,12},{6,14},{8,0},{10,2},{12,4},{14,6},{1,9},{3,11}... | collective-permute-start | bytes 196616 | tf_op jit(solution)/shard_map/ppermute | solution.py:18
  21.4 2.7 %collective-permute-start.7 = (bf16[128,256]{1,0:T(8,128)(2,1)S(1)}, bf16[128,256]{1,0:T(8,128)(2,1)S(1)}, u32[]{:S(2)}, u32[]{:S(2)}) collective-permute-start(bf16[128,256]{1,0:T(8,128)(2,1)S(1)} %fusion.39), channel_id=1, source_target_pairs={{0,8},{2,10},{4,12},{6,14},{8,0},{10,2},{12,4},{14,6},{1,9},{3,11}... | collective-permute-start | bytes 196616 | tf_op jit(solution)/shard_map/ppermute | solution.py:18
  24.4 3.0 %collective-permute-done.17 = bf16[128,256]{1,0:T(8,128)(2,1)S(1)} collective-permute-done((bf16[128,256]{1,0:T(8,128)(2,1)S(1)}, bf16[128,256]{1,0:T(8,128)(2,1)S(1)}, u32[]{:S(2)}, u32[]{:S(2)}) %collective-permute-start.17) | collective-permute-done | bytes 65568 | tf_op jit(solution)/shard_map/ppermute | solution.py:18
  27.6 2.0 %collective-permute-done.12 = bf16[128,256]{1,0:T(8,128)(2,1)S(1)} collective-permute-done((bf16[128,256]{1,0:T(8,128)(2,1)S(1)}, bf16[128,256]{1,0:T(8,128)(2,1)S(1)}, u32[]{:S(2)}, u32[]{:S(2)}) %collective-permute-start.12) | collective-permute-done | bytes 65568 | tf_op jit(solution)/shard_map/ppermute | solution.py:18
  29.8 0.5 collective-permute-done.7
  30.4 0.7 collective-permute-done.2
  31.1 1.1 %collective-permute-start.3 = (bf16[128,256]{1,0:T(8,128)(2,1)S(1)}, bf16[128,256]{1,0:T(8,128)(2,1)S(1)}, u32[]{:S(2)}, u32[]{:S(2)}) collective-permute-start(bf16[128,256]{1,0:T(8,128)(2,1)S(1)} %multiply_convert_fusion.3), channel_id=1, source_target_pairs={{0,2},{2,0},{4,6},{6,4},{8,10},{10,8},{12,14},{14,12},{1,3},{3,1},... | collective-permute-start | bytes 196616 | tf_op jit(solution)/shard_map/ppermute | solution.py:18
  32.4 0.9 %collective-permute-start.19 = (bf16[128,512]{1,0:T(8,128)(2,1)S(1)}, bf16[128,512]{1,0:T(8,128)(2,1)S(1)}, u32[]{:S(2)}, u32[]{:S(2)}) collective-permute-start(bf16[128,512]{1,0:T(8,128)(2,1)S(1)} %pad_maximum_fusion.4), channel_id=1, source_target_pairs={{0,2},{2,0},{4,6},{6,4},{8,10},{10,8},{12,14},{14,12},{1,3},{3,1},... | collective-permute-start | bytes 393224 | tf_op jit(solution)/shard_map/ppermute | solution.py:18
  33.3 1.2 %collective-permute-done.13 = bf16[128,256]{1,0:T(8,128)(2,1)S(1)} collective-permute-done((bf16[128,256]{1,0:T(8,128)(2,1)S(1)}, bf16[128,256]{1,0:T(8,128)(2,1)S(1)}, u32[]{:S(2)}, u32[]{:S(2)}) %collective-permute-start.13) | collective-permute-done | bytes 65568 | tf_op jit(solution)/shard_map/ppermute | solution.py:18
  35.3 1.6 %collective-permute-start.9 = (bf16[128,512]{1,0:T(8,128)(2,1)S(1)}, bf16[128,512]{1,0:T(8,128)(2,1)S(1)}, u32[]{:S(2)}, u32[]{:S(2)}) collective-permute-start(bf16[128,512]{1,0:T(8,128)(2,1)S(1)} %pad_maximum_fusion.2), channel_id=1, source_target_pairs={{0,2},{2,0},{4,6},{6,4},{8,10},{10,8},{12,14},{14,12},{1,3},{3,1},... | collective-permute-start | bytes 393224 | tf_op jit(solution)/shard_map/ppermute | solution.py:18
  36.9 0.7 collective-permute-start.4
  37.6 1.3 %collective-permute-done.19 = bf16[128,512]{1,0:T(8,128)(2,1)S(1)} collective-permute-done((bf16[128,512]{1,0:T(8,128)(2,1)S(1)}, bf16[128,512]{1,0:T(8,128)(2,1)S(1)}, u32[]{:S(2)}, u32[]{:S(2)}) %collective-permute-start.19) | collective-permute-done | bytes 131104 | tf_op jit(solution)/shard_map/ppermute | solution.py:18
  40.8 1.1 %collective-permute-done.4 = bf16[128,512]{1,0:T(8,128)(2,1)S(1)} collective-permute-done((bf16[128,512]{1,0:T(8,128)(2,1)S(1)}, bf16[128,512]{1,0:T(8,128)(2,1)S(1)}, u32[]{:S(2)}, u32[]{:S(2)}) %collective-permute-start.4) | collective-permute-done | bytes 131104 | tf_op jit(solution)/shard_map/ppermute | solution.py:18
  42.5 1.5 %collective-permute-done.20.other_ref = f32[512,128]{1,0:T(8,128)S(1)} collective-permute-done((f32[512,128]{1,0:T(8,128)S(1)}, f32[512,128]{1,0:T(8,128)S(1)}, u32[]{:S(2)}, u32[]{:S(2)}) %collective-permute-start.20) | collective-permute-done | bytes 262176 | tf_op jit(solution)/shard_map/ppermute | solution.py:18
  44.0 0.5 make_gram.1
  44.5 1.7 %collective-permute-start.24 = (f32[72,128]{1,0:T(8,128)S(1)}, f32[72,128]{1,0:T(8,128)S(1)}, u32[]{:S(2)}, u32[]{:S(2)}) collective-permute-start(f32[72,128]{1,0:T(8,128)S(1)} %get-tuple-element.17), channel_id=1, source_target_pairs={{0,10},{1,15},{2,8},{3,13},{4,14},{5,11},{6,12},{7,9},{8,2},{9,7},... | collective-permute-start | bytes 110600 | tf_op jit(solution)/shard_map/ppermute | solution.py:36
  46.3 1.2 %collective-permute-start.23 = (f32[72,128]{1,0:T(8,128)S(1)}, f32[72,128]{1,0:T(8,128)S(1)}, u32[]{:S(2)}, u32[]{:S(2)}) collective-permute-start(f32[72,128]{1,0:T(8,128)S(1)} %get-tuple-element.17), channel_id=1, source_target_pairs={{0,8},{1,13},{2,10},{3,15},{4,12},{5,9},{6,14},{7,11},{8,0},{9,5},... | collective-permute-start | bytes 110600 | tf_op jit(solution)/shard_map/ppermute | solution.py:36
  47.5 1.5 %collective-permute-start.22 = (f32[72,128]{1,0:T(8,128)S(1)}, f32[72,128]{1,0:T(8,128)S(1)}, u32[]{:S(2)}, u32[]{:S(2)}) collective-permute-start(f32[72,128]{1,0:T(8,128)S(1)} %get-tuple-element.17), channel_id=1, source_target_pairs={{0,2},{1,7},{2,0},{3,5},{4,6},{5,3},{6,4},{7,1},{8,10},{9,15},{10,... | collective-permute-start | bytes 110600 | tf_op jit(solution)/shard_map/ppermute | solution.py:36
  49.0 0.7 collective-permute-start.21
  49.7 1.5 %collective-permute-done.24 = f32[72,128]{1,0:T(8,128)S(1)} collective-permute-done((f32[72,128]{1,0:T(8,128)S(1)}, f32[72,128]{1,0:T(8,128)S(1)}, u32[]{:S(2)}, u32[]{:S(2)}) %collective-permute-start.24) | collective-permute-done | bytes 36896 | tf_op jit(solution)/shard_map/ppermute | solution.py:36
  51.2 0.9 %collective-permute-done.23 = f32[72,128]{1,0:T(8,128)S(1)} collective-permute-done((f32[72,128]{1,0:T(8,128)S(1)}, f32[72,128]{1,0:T(8,128)S(1)}, u32[]{:S(2)}, u32[]{:S(2)}) %collective-permute-start.23) | collective-permute-done | bytes 36896 | tf_op jit(solution)/shard_map/ppermute | solution.py:36
  52.0 1.6 %collective-permute-start.25 = (f32[72,128]{1,0:T(8,128)S(1)}, f32[72,128]{1,0:T(8,128)S(1)}, u32[]{:S(2)}, u32[]{:S(2)}) collective-permute-start(f32[72,128]{1,0:T(8,128)S(1)} %add_add_fusion), channel_id=1, source_target_pairs={{0,1},{1,0},{2,3},{3,2},{4,5},{5,4},{6,7},{7,6},{8,9},{9,8},{10,11... | collective-permute-start | bytes 110600 | tf_op jit(solution)/shard_map/ppermute | solution.py:18
  53.7 0.9 %collective-permute-done.25 = f32[72,128]{1,0:T(8,128)S(1)} collective-permute-done((f32[72,128]{1,0:T(8,128)S(1)}, f32[72,128]{1,0:T(8,128)S(1)}, u32[]{:S(2)}, u32[]{:S(2)}) %collective-permute-start.25) | collective-permute-done | bytes 36896 | tf_op jit(solution)/shard_map/ppermute | solution.py:18
  54.6 4.1 %make_basis.1 = (f32[512,128]{1,0:T(8,128)}, f32[128,1024]{1,0:T(8,128)S(1)}, f32[128,1024]{1,0:T(8,128)S(1)}, f32[128,1024]{1,0:T(8,128)S(1)}, f32[128,1024]{1,0:T(8,128)S(1)}) custom-call(f32[72,128]{1,0:T(8,128)S(1)} %add.116.gram_ref, f32[128,512]{1,0:T(8,128)S(1)} %get-tuple-element.18.sketch_ref, bf16[512,4096]{1,0:T(8,128)(2,1)} %slab_ref.5), custom_call_target="tpu_custom_call" | custom-call | tf_op jit(solution)/shard_map/make_basis/pallas_call | solution.py:279
  58.8 0.6 collective-permute-start.26
  59.5 1.7 %collective-permute-start.29 = (bf16[2,2,16,1024]{3,2,0,1:T(8,128)(2,1)S(1)}, bf16[2,2,16,1024]{3,2,0,1:T(8,128)(2,1)S(1)}, u32[]{:S(2)}, u32[]{:S(2)}) collective-permute-start(bf16[2,2,16,1024]{3,2,0,1:T(8,128)(2,1)S(1)} %fusion.23), channel_id=1, source_target_pairs={{0,4},{2,6},{4,0},{6,2},{8,12},{10,14},{12,8},{14,10},{1,5},{3,7},... | collective-permute-start | bytes 393224 | tf_op jit(solution)/shard_map/ppermute | solution.py:18
  61.3 1.6 %collective-permute-start.32 = (bf16[2,2,16,1024]{3,2,0,1:T(8,128)(2,1)S(1)}, bf16[2,2,16,1024]{3,2,0,1:T(8,128)(2,1)S(1)}, u32[]{:S(2)}, u32[]{:S(2)}) collective-permute-start(bf16[2,2,16,1024]{3,2,0,1:T(8,128)(2,1)S(1)} %fusion.24), channel_id=1, source_target_pairs={{0,2},{2,0},{4,6},{6,4},{8,10},{10,8},{12,14},{14,12},{1,3},{3,1},... | collective-permute-start | bytes 393224 | tf_op jit(solution)/shard_map/ppermute | solution.py:18
  63.3 1.8 %collective-permute-done.26 = bf16[2,2,16,1024]{3,2,0,1:T(8,128)(2,1)S(1)} collective-permute-done((bf16[2,2,16,1024]{3,2,0,1:T(8,128)(2,1)S(1)}, bf16[2,2,16,1024]{3,2,0,1:T(8,128)(2,1)S(1)}, u32[]{:S(2)}, u32[]{:S(2)}) %collective-permute-start.26) | collective-permute-done | bytes 131104 | tf_op jit(solution)/shard_map/ppermute | solution.py:18
  65.2 1.8 %collective-permute-start.27 = (bf16[2,16,1024]{2,1,0:T(8,128)(2,1)S(1)}, bf16[2,16,1024]{2,1,0:T(8,128)(2,1)S(1)}, u32[]{:S(2)}, u32[]{:S(2)}) collective-permute-start(bf16[2,16,1024]{2,1,0:T(8,128)(2,1)S(1)} %fusion.26), channel_id=1, source_target_pairs={{0,4},{2,6},{4,0},{6,2},{8,12},{10,14},{12,8},{14,10},{1,5},{3,7},... | collective-permute-start | bytes 196616 | tf_op jit(solution)/shard_map/ppermute | solution.py:18
  67.1 0.6 collective-permute-start.30
  67.7 1.8 %collective-permute-start.33 = (bf16[2,16,1024]{2,1,0:T(8,128)(2,1)S(1)}, bf16[2,16,1024]{2,1,0:T(8,128)(2,1)S(1)}, u32[]{:S(2)}, u32[]{:S(2)}) collective-permute-start(bf16[2,16,1024]{2,1,0:T(8,128)(2,1)S(1)} %fusion.28), channel_id=1, source_target_pairs={{0,4},{2,6},{4,0},{6,2},{8,12},{10,14},{12,8},{14,10},{1,5},{3,7},... | collective-permute-start | bytes 196616 | tf_op jit(solution)/shard_map/ppermute | solution.py:18
  70.1 1.9 %collective-permute-start.28 = (bf16[16,1024]{1,0:T(8,128)(2,1)S(1)}, bf16[16,1024]{1,0:T(8,128)(2,1)S(1)}, u32[]{:S(2)}, u32[]{:S(2)}) collective-permute-start(bf16[16,1024]{1,0:T(8,128)(2,1)S(1)} %fusion.34), channel_id=1, source_target_pairs={{0,8},{2,10},{4,12},{6,14},{8,0},{10,2},{12,4},{14,6},{1,9},{3,11}... | collective-permute-start | bytes 98312 | tf_op jit(solution)/shard_map/ppermute | solution.py:18
  72.1 1.1 %collective-permute-start.31 = (bf16[16,1024]{1,0:T(8,128)(2,1)S(1)}, bf16[16,1024]{1,0:T(8,128)(2,1)S(1)}, u32[]{:S(2)}, u32[]{:S(2)}) collective-permute-start(bf16[16,1024]{1,0:T(8,128)(2,1)S(1)} %fusion.35), channel_id=1, source_target_pairs={{0,8},{2,10},{4,12},{6,14},{8,0},{10,2},{12,4},{14,6},{1,9},{3,11}... | collective-permute-start | bytes 98312 | tf_op jit(solution)/shard_map/ppermute | solution.py:18
  73.3 1.9 %collective-permute-start.34 = (bf16[16,1024]{1,0:T(8,128)(2,1)S(1)}, bf16[16,1024]{1,0:T(8,128)(2,1)S(1)}, u32[]{:S(2)}, u32[]{:S(2)}) collective-permute-start(bf16[16,1024]{1,0:T(8,128)(2,1)S(1)} %fusion.36), channel_id=1, source_target_pairs={{0,8},{2,10},{4,12},{6,14},{8,0},{10,2},{12,4},{14,6},{1,9},{3,11}... | collective-permute-start | bytes 98312 | tf_op jit(solution)/shard_map/ppermute | solution.py:18
  75.3 1.1 %collective-permute-start.37 = (bf16[16,1024]{1,0:T(8,128)(2,1)S(1)}, bf16[16,1024]{1,0:T(8,128)(2,1)S(1)}, u32[]{:S(2)}, u32[]{:S(2)}) collective-permute-start(bf16[16,1024]{1,0:T(8,128)(2,1)S(1)} %fusion.37), channel_id=1, source_target_pairs={{0,8},{2,10},{4,12},{6,14},{8,0},{10,2},{12,4},{14,6},{1,9},{3,11}... | collective-permute-start | bytes 98312 | tf_op jit(solution)/shard_map/ppermute | solution.py:18
  76.4 1.5 %collective-permute-done.31 = bf16[16,1024]{1,0:T(8,128)(2,1)S(1)} collective-permute-done((bf16[16,1024]{1,0:T(8,128)(2,1)S(1)}, bf16[16,1024]{1,0:T(8,128)(2,1)S(1)}, u32[]{:S(2)}, u32[]{:S(2)}) %collective-permute-start.31) | collective-permute-done | bytes 32800 | tf_op jit(solution)/shard_map/ppermute | solution.py:18
  78.4 2.1 %collective-permute-done.37 = bf16[16,1024]{1,0:T(8,128)(2,1)S(1)} collective-permute-done((bf16[16,1024]{1,0:T(8,128)(2,1)S(1)}, bf16[16,1024]{1,0:T(8,128)(2,1)S(1)}, u32[]{:S(2)}, u32[]{:S(2)}) %collective-permute-start.37) | collective-permute-done | bytes 32800 | tf_op jit(solution)/shard_map/ppermute | solution.py:18
  80.5 0.7 pad_maximum_fusion
  (105 shorter events, 7.8 us)
Async XLA Ops:
  0.6 0.9 %copy-start = (bf16[512,128]{1,0:T(8,128)(2,1)S(1)}, bf16[512,128]{1,0:T(8,128)(2,1)}, u32[]{:S(2)}) copy-start(bf16[512,128]{1,0:T(8,128)(2,1)} %start_ref.3) | copy-start | bytes 393220
  1.5 6.6 %copy-start.1 = (bf16[512,128]{1,0:T(8,128)(2,1)S(1)}, bf16[512,128]{1,0:T(8,128)(2,1)}, u32[]{:S(2)}) copy-start(bf16[512,128]{1,0:T(8,128)(2,1)} %start_ref.3) | copy-start | bytes 393220
  3.5 7.3 %collective-permute-start.15 = (bf16[128,512]{1,0:T(8,128)(2,1)S(1)}, bf16[128,512]{1,0:T(8,128)(2,1)S(1)}, u32[]{:S(2)}, u32[]{:S(2)}) collective-permute-start(bf16[128,512]{1,0:T(8,128)(2,1)S(1)} %select_convert_fusion.4), channel_id=1, source_target_pairs={{0,2},{2,0},{4,6},{6,4},{8,10},{10,8},{12,14},{14,12},{1,3},{3,1},... | collective-permute-start | bytes 393224 | tf_op jit(solution)/shard_map/ppermute | solution.py:18
  6.5 6.4 %collective-permute-start.10 = (bf16[128,512]{1,0:T(8,128)(2,1)S(1)}, bf16[128,512]{1,0:T(8,128)(2,1)S(1)}, u32[]{:S(2)}, u32[]{:S(2)}) collective-permute-start(bf16[128,512]{1,0:T(8,128)(2,1)S(1)} %select_convert_fusion.5), channel_id=1, source_target_pairs={{0,4},{2,6},{4,0},{6,2},{8,12},{10,14},{12,8},{14,10},{1,5},{3,7},... | collective-permute-start | bytes 393224 | tf_op jit(solution)/shard_map/ppermute | solution.py:18
  10.1 5.7 %collective-permute-start.5 = (bf16[128,512]{1,0:T(8,128)(2,1)S(1)}, bf16[128,512]{1,0:T(8,128)(2,1)S(1)}, u32[]{:S(2)}, u32[]{:S(2)}) collective-permute-start(bf16[128,512]{1,0:T(8,128)(2,1)S(1)} %select_convert_fusion.6), channel_id=1, source_target_pairs={{0,2},{2,0},{4,6},{6,4},{8,10},{10,8},{12,14},{14,12},{1,3},{3,1},... | collective-permute-start | bytes 393224 | tf_op jit(solution)/shard_map/ppermute | solution.py:18
  10.7 5.7 %collective-permute-start = (bf16[128,512]{1,0:T(8,128)(2,1)S(1)}, bf16[128,512]{1,0:T(8,128)(2,1)S(1)}, u32[]{:S(2)}, u32[]{:S(2)}) collective-permute-start(bf16[128,512]{1,0:T(8,128)(2,1)S(1)} %select_convert_fusion.7), channel_id=1, source_target_pairs={{0,4},{2,6},{4,0},{6,2},{8,12},{10,14},{12,8},{14,10},{1,5},{3,7},... | collective-permute-start | bytes 393224 | tf_op jit(solution)/shard_map/ppermute | solution.py:18
  10.9 7.3 %collective-permute-start.16 = (bf16[128,256]{1,0:T(8,128)(2,1)S(1)}, bf16[128,256]{1,0:T(8,128)(2,1)S(1)}, u32[]{:S(2)}, u32[]{:S(2)}) collective-permute-start(bf16[128,256]{1,0:T(8,128)(2,1)S(1)} %select_convert_fusion.12), channel_id=1, source_target_pairs={{0,4},{2,6},{4,0},{6,2},{8,12},{10,14},{12,8},{14,10},{1,5},{3,7},... | collective-permute-start | bytes 196616 | tf_op jit(solution)/shard_map/ppermute | solution.py:18
  13.0 25.9 %copy-start.2 = (bf16[512,4096]{1,0:T(8,128)(2,1)S(1)}, bf16[512,4096]{1,0:T(8,128)(2,1)}, u32[]{:S(2)}) copy-start(bf16[512,4096]{1,0:T(8,128)(2,1)} %slab_ref.5) | copy-start | bytes 12582916
  13.0 7.9 %collective-permute-start.11 = (bf16[128,256]{1,0:T(8,128)(2,1)S(1)}, bf16[128,256]{1,0:T(8,128)(2,1)S(1)}, u32[]{:S(2)}, u32[]{:S(2)}) collective-permute-start(bf16[128,256]{1,0:T(8,128)(2,1)S(1)} %select_convert_fusion.13), channel_id=1, source_target_pairs={{0,2},{2,0},{4,6},{6,4},{8,10},{10,8},{12,14},{14,12},{1,3},{3,1},... | collective-permute-start | bytes 196616 | tf_op jit(solution)/shard_map/ppermute | solution.py:18
  15.9 5.4 %collective-permute-start.6 = (bf16[128,256]{1,0:T(8,128)(2,1)S(1)}, bf16[128,256]{1,0:T(8,128)(2,1)S(1)}, u32[]{:S(2)}, u32[]{:S(2)}) collective-permute-start(bf16[128,256]{1,0:T(8,128)(2,1)S(1)} %select_convert_fusion.14), channel_id=1, source_target_pairs={{0,4},{2,6},{4,0},{6,2},{8,12},{10,14},{12,8},{14,10},{1,5},{3,7},... | collective-permute-start | bytes 196616 | tf_op jit(solution)/shard_map/ppermute | solution.py:18
  16.5 7.5 %collective-permute-start.1 = (bf16[128,256]{1,0:T(8,128)(2,1)S(1)}, bf16[128,256]{1,0:T(8,128)(2,1)S(1)}, u32[]{:S(2)}, u32[]{:S(2)}) collective-permute-start(bf16[128,256]{1,0:T(8,128)(2,1)S(1)} %select_convert_fusion.15), channel_id=1, source_target_pairs={{0,2},{2,0},{4,6},{6,4},{8,10},{10,8},{12,14},{14,12},{1,3},{3,1},... | collective-permute-start | bytes 196616 | tf_op jit(solution)/shard_map/ppermute | solution.py:18
  18.2 9.2 %collective-permute-start.17 = (bf16[128,256]{1,0:T(8,128)(2,1)S(1)}, bf16[128,256]{1,0:T(8,128)(2,1)S(1)}, u32[]{:S(2)}, u32[]{:S(2)}) collective-permute-start(bf16[128,256]{1,0:T(8,128)(2,1)S(1)} %fusion.41), channel_id=1, source_target_pairs={{0,8},{2,10},{4,12},{6,14},{8,0},{10,2},{12,4},{14,6},{1,9},{3,11}... | collective-permute-start | bytes 196616 | tf_op jit(solution)/shard_map/ppermute | solution.py:18
  20.9 8.6 %collective-permute-start.12 = (bf16[128,256]{1,0:T(8,128)(2,1)S(1)}, bf16[128,256]{1,0:T(8,128)(2,1)S(1)}, u32[]{:S(2)}, u32[]{:S(2)}) collective-permute-start(bf16[128,256]{1,0:T(8,128)(2,1)S(1)} %fusion.40), channel_id=1, source_target_pairs={{0,8},{2,10},{4,12},{6,14},{8,0},{10,2},{12,4},{14,6},{1,9},{3,11}... | collective-permute-start | bytes 196616 | tf_op jit(solution)/shard_map/ppermute | solution.py:18
  21.4 8.9 %collective-permute-start.7 = (bf16[128,256]{1,0:T(8,128)(2,1)S(1)}, bf16[128,256]{1,0:T(8,128)(2,1)S(1)}, u32[]{:S(2)}, u32[]{:S(2)}) collective-permute-start(bf16[128,256]{1,0:T(8,128)(2,1)S(1)} %fusion.39), channel_id=1, source_target_pairs={{0,8},{2,10},{4,12},{6,14},{8,0},{10,2},{12,4},{14,6},{1,9},{3,11}... | collective-permute-start | bytes 196616 | tf_op jit(solution)/shard_map/ppermute | solution.py:18
  24.1 7.0 %collective-permute-start.2 = (bf16[128,256]{1,0:T(8,128)(2,1)S(1)}, bf16[128,256]{1,0:T(8,128)(2,1)S(1)}, u32[]{:S(2)}, u32[]{:S(2)}) collective-permute-start(bf16[128,256]{1,0:T(8,128)(2,1)S(1)} %fusion.38), channel_id=1, source_target_pairs={{0,8},{2,10},{4,12},{6,14},{8,0},{10,2},{12,4},{14,6},{1,9},{3,11}... | collective-permute-start | bytes 196616 | tf_op jit(solution)/shard_map/ppermute | solution.py:18
  27.5 4.9 %collective-permute-start.18 = (bf16[128,256]{1,0:T(8,128)(2,1)S(1)}, bf16[128,256]{1,0:T(8,128)(2,1)S(1)}, u32[]{:S(2)}, u32[]{:S(2)}) collective-permute-start(bf16[128,256]{1,0:T(8,128)(2,1)S(1)} %multiply_convert_fusion), channel_id=1, source_target_pairs={{0,4},{2,6},{4,0},{6,2},{8,12},{10,14},{12,8},{14,10},{1,5},{3,7},... | collective-permute-start | bytes 196616 | tf_op jit(solution)/shard_map/ppermute | solution.py:18
  29.6 4.8 %collective-permute-start.13 = (bf16[128,256]{1,0:T(8,128)(2,1)S(1)}, bf16[128,256]{1,0:T(8,128)(2,1)S(1)}, u32[]{:S(2)}, u32[]{:S(2)}) collective-permute-start(bf16[128,256]{1,0:T(8,128)(2,1)S(1)} %multiply_convert_fusion.1), channel_id=1, source_target_pairs={{0,2},{2,0},{4,6},{6,4},{8,10},{10,8},{12,14},{14,12},{1,3},{3,1},... | collective-permute-start | bytes 196616 | tf_op jit(solution)/shard_map/ppermute | solution.py:18
  30.3 4.9 %collective-permute-start.8 = (bf16[128,256]{1,0:T(8,128)(2,1)S(1)}, bf16[128,256]{1,0:T(8,128)(2,1)S(1)}, u32[]{:S(2)}, u32[]{:S(2)}) collective-permute-start(bf16[128,256]{1,0:T(8,128)(2,1)S(1)} %multiply_convert_fusion.2), channel_id=1, source_target_pairs={{0,4},{2,6},{4,0},{6,2},{8,12},{10,14},{12,8},{14,10},{1,5},{3,7},... | collective-permute-start | bytes 196616 | tf_op jit(solution)/shard_map/ppermute | solution.py:18
  31.1 5.8 %collective-permute-start.3 = (bf16[128,256]{1,0:T(8,128)(2,1)S(1)}, bf16[128,256]{1,0:T(8,128)(2,1)S(1)}, u32[]{:S(2)}, u32[]{:S(2)}) collective-permute-start(bf16[128,256]{1,0:T(8,128)(2,1)S(1)} %multiply_convert_fusion.3), channel_id=1, source_target_pairs={{0,2},{2,0},{4,6},{6,4},{8,10},{10,8},{12,14},{14,12},{1,3},{3,1},... | collective-permute-start | bytes 196616 | tf_op jit(solution)/shard_map/ppermute | solution.py:18
  32.4 6.4 %collective-permute-start.19 = (bf16[128,512]{1,0:T(8,128)(2,1)S(1)}, bf16[128,512]{1,0:T(8,128)(2,1)S(1)}, u32[]{:S(2)}, u32[]{:S(2)}) collective-permute-start(bf16[128,512]{1,0:T(8,128)(2,1)S(1)} %pad_maximum_fusion.4), channel_id=1, source_target_pairs={{0,2},{2,0},{4,6},{6,4},{8,10},{10,8},{12,14},{14,12},{1,3},{3,1},... | collective-permute-start | bytes 393224 | tf_op jit(solution)/shard_map/ppermute | solution.py:18
  34.5 5.0 %collective-permute-start.14 = (bf16[128,512]{1,0:T(8,128)(2,1)S(1)}, bf16[128,512]{1,0:T(8,128)(2,1)S(1)}, u32[]{:S(2)}, u32[]{:S(2)}) collective-permute-start(bf16[128,512]{1,0:T(8,128)(2,1)S(1)} %pad_maximum_fusion.3), channel_id=1, source_target_pairs={{0,4},{2,6},{4,0},{6,2},{8,12},{10,14},{12,8},{14,10},{1,5},{3,7},... | collective-permute-start | bytes 393224 | tf_op jit(solution)/shard_map/ppermute | solution.py:18
  35.3 5.0 %collective-permute-start.9 = (bf16[128,512]{1,0:T(8,128)(2,1)S(1)}, bf16[128,512]{1,0:T(8,128)(2,1)S(1)}, u32[]{:S(2)}, u32[]{:S(2)}) collective-permute-start(bf16[128,512]{1,0:T(8,128)(2,1)S(1)} %pad_maximum_fusion.2), channel_id=1, source_target_pairs={{0,2},{2,0},{4,6},{6,4},{8,10},{10,8},{12,14},{14,12},{1,3},{3,1},... | collective-permute-start | bytes 393224 | tf_op jit(solution)/shard_map/ppermute | solution.py:18
  36.9 5.0 %collective-permute-start.4 = (bf16[128,512]{1,0:T(8,128)(2,1)S(1)}, bf16[128,512]{1,0:T(8,128)(2,1)S(1)}, u32[]{:S(2)}, u32[]{:S(2)}) collective-permute-start(bf16[128,512]{1,0:T(8,128)(2,1)S(1)} %pad_maximum_fusion.1), channel_id=1, source_target_pairs={{0,4},{2,6},{4,0},{6,2},{8,12},{10,14},{12,8},{14,10},{1,5},{3,7},... | collective-permute-start | bytes 393224 | tf_op jit(solution)/shard_map/ppermute | solution.py:18
  42.4 1.6 %collective-permute-start.20 = (f32[512,128]{1,0:T(8,128)S(1)}, f32[512,128]{1,0:T(8,128)S(1)}, u32[]{:S(2)}, u32[]{:S(2)}) collective-permute-start(f32[512,128]{1,0:T(8,128)S(1)} %fusion.2.mine_ref), channel_id=1, source_target_pairs={{0,1},{1,0},{2,3},{3,2},{4,5},{5,4},{6,7},{7,6},{8,9},{9,8},{10,11... | collective-permute-start | bytes 786440 | tf_op jit(solution)/shard_map/ppermute | solution.py:18
  44.5 6.6 %collective-permute-start.24 = (f32[72,128]{1,0:T(8,128)S(1)}, f32[72,128]{1,0:T(8,128)S(1)}, u32[]{:S(2)}, u32[]{:S(2)}) collective-permute-start(f32[72,128]{1,0:T(8,128)S(1)} %get-tuple-element.17), channel_id=1, source_target_pairs={{0,10},{1,15},{2,8},{3,13},{4,14},{5,11},{6,12},{7,9},{8,2},{9,7},... | collective-permute-start | bytes 110600 | tf_op jit(solution)/shard_map/ppermute | solution.py:36
  46.3 5.7 %collective-permute-start.23 = (f32[72,128]{1,0:T(8,128)S(1)}, f32[72,128]{1,0:T(8,128)S(1)}, u32[]{:S(2)}, u32[]{:S(2)}) collective-permute-start(f32[72,128]{1,0:T(8,128)S(1)} %get-tuple-element.17), channel_id=1, source_target_pairs={{0,8},{1,13},{2,10},{3,15},{4,12},{5,9},{6,14},{7,11},{8,0},{9,5},... | collective-permute-start | bytes 110600 | tf_op jit(solution)/shard_map/ppermute | solution.py:36
  47.5 4.6 %collective-permute-start.22 = (f32[72,128]{1,0:T(8,128)S(1)}, f32[72,128]{1,0:T(8,128)S(1)}, u32[]{:S(2)}, u32[]{:S(2)}) collective-permute-start(f32[72,128]{1,0:T(8,128)S(1)} %get-tuple-element.17), channel_id=1, source_target_pairs={{0,2},{1,7},{2,0},{3,5},{4,6},{5,3},{6,4},{7,1},{8,10},{9,15},{10,... | collective-permute-start | bytes 110600 | tf_op jit(solution)/shard_map/ppermute | solution.py:36
  49.0 3.0 %collective-permute-start.21 = (f32[72,128]{1,0:T(8,128)S(1)}, f32[72,128]{1,0:T(8,128)S(1)}, u32[]{:S(2)}, u32[]{:S(2)}) collective-permute-start(f32[72,128]{1,0:T(8,128)S(1)} %get-tuple-element.17), channel_id=1, source_target_pairs={{1,5},{3,7},{5,1},{7,3},{9,13},{11,15},{13,9},{15,11},{17,21},{19,... | collective-permute-start | bytes 110600 | tf_op jit(solution)/shard_map/ppermute | solution.py:36
  52.0 2.5 %collective-permute-start.25 = (f32[72,128]{1,0:T(8,128)S(1)}, f32[72,128]{1,0:T(8,128)S(1)}, u32[]{:S(2)}, u32[]{:S(2)}) collective-permute-start(f32[72,128]{1,0:T(8,128)S(1)} %add_add_fusion), channel_id=1, source_target_pairs={{0,1},{1,0},{2,3},{3,2},{4,5},{5,4},{6,7},{7,6},{8,9},{9,8},{10,11... | collective-permute-start | bytes 110600 | tf_op jit(solution)/shard_map/ppermute | solution.py:18
  58.8 6.4 %collective-permute-start.26 = (bf16[2,2,16,1024]{3,2,0,1:T(8,128)(2,1)S(1)}, bf16[2,2,16,1024]{3,2,0,1:T(8,128)(2,1)S(1)}, u32[]{:S(2)}, u32[]{:S(2)}) collective-permute-start(bf16[2,2,16,1024]{3,2,0,1:T(8,128)(2,1)S(1)} %fusion.22), channel_id=1, source_target_pairs={{0,2},{2,0},{4,6},{6,4},{8,10},{10,8},{12,14},{14,12},{1,3},{3,1},... | collective-permute-start | bytes 393224 | tf_op jit(solution)/shard_map/ppermute | solution.py:18
  59.5 7.6 %collective-permute-start.29 = (bf16[2,2,16,1024]{3,2,0,1:T(8,128)(2,1)S(1)}, bf16[2,2,16,1024]{3,2,0,1:T(8,128)(2,1)S(1)}, u32[]{:S(2)}, u32[]{:S(2)}) collective-permute-start(bf16[2,2,16,1024]{3,2,0,1:T(8,128)(2,1)S(1)} %fusion.23), channel_id=1, source_target_pairs={{0,4},{2,6},{4,0},{6,2},{8,12},{10,14},{12,8},{14,10},{1,5},{3,7},... | collective-permute-start | bytes 393224 | tf_op jit(solution)/shard_map/ppermute | solution.py:18
  61.3 6.4 %collective-permute-start.32 = (bf16[2,2,16,1024]{3,2,0,1:T(8,128)(2,1)S(1)}, bf16[2,2,16,1024]{3,2,0,1:T(8,128)(2,1)S(1)}, u32[]{:S(2)}, u32[]{:S(2)}) collective-permute-start(bf16[2,2,16,1024]{3,2,0,1:T(8,128)(2,1)S(1)} %fusion.24), channel_id=1, source_target_pairs={{0,2},{2,0},{4,6},{6,4},{8,10},{10,8},{12,14},{14,12},{1,3},{3,1},... | collective-permute-start | bytes 393224 | tf_op jit(solution)/shard_map/ppermute | solution.py:18
  62.9 6.6 %collective-permute-start.35 = (bf16[2,2,16,1024]{3,2,0,1:T(8,128)(2,1)S(1)}, bf16[2,2,16,1024]{3,2,0,1:T(8,128)(2,1)S(1)}, u32[]{:S(2)}, u32[]{:S(2)}) collective-permute-start(bf16[2,2,16,1024]{3,2,0,1:T(8,128)(2,1)S(1)} %fusion.25), channel_id=1, source_target_pairs={{0,4},{2,6},{4,0},{6,2},{8,12},{10,14},{12,8},{14,10},{1,5},{3,7},... | collective-permute-start | bytes 393224 | tf_op jit(solution)/shard_map/ppermute | solution.py:18
  65.2 4.9 %collective-permute-start.27 = (bf16[2,16,1024]{2,1,0:T(8,128)(2,1)S(1)}, bf16[2,16,1024]{2,1,0:T(8,128)(2,1)S(1)}, u32[]{:S(2)}, u32[]{:S(2)}) collective-permute-start(bf16[2,16,1024]{2,1,0:T(8,128)(2,1)S(1)} %fusion.26), channel_id=1, source_target_pairs={{0,4},{2,6},{4,0},{6,2},{8,12},{10,14},{12,8},{14,10},{1,5},{3,7},... | collective-permute-start | bytes 196616 | tf_op jit(solution)/shard_map/ppermute | solution.py:18
  67.1 5.0 %collective-permute-start.30 = (bf16[2,16,1024]{2,1,0:T(8,128)(2,1)S(1)}, bf16[2,16,1024]{2,1,0:T(8,128)(2,1)S(1)}, u32[]{:S(2)}, u32[]{:S(2)}) collective-permute-start(bf16[2,16,1024]{2,1,0:T(8,128)(2,1)S(1)} %fusion.27), channel_id=1, source_target_pairs={{0,2},{2,0},{4,6},{6,4},{8,10},{10,8},{12,14},{14,12},{1,3},{3,1},... | collective-permute-start | bytes 196616 | tf_op jit(solution)/shard_map/ppermute | solution.py:18
  67.7 5.5 %collective-permute-start.33 = (bf16[2,16,1024]{2,1,0:T(8,128)(2,1)S(1)}, bf16[2,16,1024]{2,1,0:T(8,128)(2,1)S(1)}, u32[]{:S(2)}, u32[]{:S(2)}) collective-permute-start(bf16[2,16,1024]{2,1,0:T(8,128)(2,1)S(1)} %fusion.28), channel_id=1, source_target_pairs={{0,4},{2,6},{4,0},{6,2},{8,12},{10,14},{12,8},{14,10},{1,5},{3,7},... | collective-permute-start | bytes 196616 | tf_op jit(solution)/shard_map/ppermute | solution.py:18
  69.6 5.6 %collective-permute-start.36 = (bf16[2,16,1024]{2,1,0:T(8,128)(2,1)S(1)}, bf16[2,16,1024]{2,1,0:T(8,128)(2,1)S(1)}, u32[]{:S(2)}, u32[]{:S(2)}) collective-permute-start(bf16[2,16,1024]{2,1,0:T(8,128)(2,1)S(1)} %fusion.29), channel_id=1, source_target_pairs={{0,2},{2,0},{4,6},{6,4},{8,10},{10,8},{12,14},{14,12},{1,3},{3,1},... | collective-permute-start | bytes 196616 | tf_op jit(solution)/shard_map/ppermute | solution.py:18
  70.1 6.3 %collective-permute-start.28 = (bf16[16,1024]{1,0:T(8,128)(2,1)S(1)}, bf16[16,1024]{1,0:T(8,128)(2,1)S(1)}, u32[]{:S(2)}, u32[]{:S(2)}) collective-permute-start(bf16[16,1024]{1,0:T(8,128)(2,1)S(1)} %fusion.34), channel_id=1, source_target_pairs={{0,8},{2,10},{4,12},{6,14},{8,0},{10,2},{12,4},{14,6},{1,9},{3,11}... | collective-permute-start | bytes 98312 | tf_op jit(solution)/shard_map/ppermute | solution.py:18
  72.1 5.8 %collective-permute-start.31 = (bf16[16,1024]{1,0:T(8,128)(2,1)S(1)}, bf16[16,1024]{1,0:T(8,128)(2,1)S(1)}, u32[]{:S(2)}, u32[]{:S(2)}) collective-permute-start(bf16[16,1024]{1,0:T(8,128)(2,1)S(1)} %fusion.35), channel_id=1, source_target_pairs={{0,8},{2,10},{4,12},{6,14},{8,0},{10,2},{12,4},{14,6},{1,9},{3,11}... | collective-permute-start | bytes 98312 | tf_op jit(solution)/shard_map/ppermute | solution.py:18
  73.3 5.1 %collective-permute-start.34 = (bf16[16,1024]{1,0:T(8,128)(2,1)S(1)}, bf16[16,1024]{1,0:T(8,128)(2,1)S(1)}, u32[]{:S(2)}, u32[]{:S(2)}) collective-permute-start(bf16[16,1024]{1,0:T(8,128)(2,1)S(1)} %fusion.36), channel_id=1, source_target_pairs={{0,8},{2,10},{4,12},{6,14},{8,0},{10,2},{12,4},{14,6},{1,9},{3,11}... | collective-permute-start | bytes 98312 | tf_op jit(solution)/shard_map/ppermute | solution.py:18
  75.3 5.2 %collective-permute-start.37 = (bf16[16,1024]{1,0:T(8,128)(2,1)S(1)}, bf16[16,1024]{1,0:T(8,128)(2,1)S(1)}, u32[]{:S(2)}, u32[]{:S(2)}) collective-permute-start(bf16[16,1024]{1,0:T(8,128)(2,1)S(1)} %fusion.37), channel_id=1, source_target_pairs={{0,8},{2,10},{4,12},{6,14},{8,0},{10,2},{12,4},{14,6},{1,9},{3,11}... | collective-permute-start | bytes 98312 | tf_op jit(solution)/shard_map/ppermute | solution.py:18
